TPU v7x, 32 devices: a whole 2x2x4 slice. The times are simulated.
32 devices in a mesh: row: 4 (over z), col: 8 (over y, x, core).
Axes of the slice: x: 2, y: 2, z: 4, core: 2. Of those that a mesh axis runs over, the one named last changes fastest.
Arguments:
- tiles: bfloat16 [4, 8, 32, 128, 128], P('row', 'col'), may hold values from 1.347065e-05 to 0.013427734
- tile_rows: int32 [4, 8, 32], P('row', 'col'), may hold values from 0 to 63, as said below
- tile_cols: int32 [4, 8, 32], P('row', 'col'), may hold values from 0 to 31, as said below
- start_vectors: float32 [64, 32768], P(None, ('row', 'col')), may hold values from -6 to 6
Outputs:
- ritz: float32 [64, 32768], P(None, ('row', 'col'))
- rayleigh: float32 [64, 64], replicated
Inputs may be any that keep to these rules, and one draw needn't show every extreme that they name: `tile_rows`: tile row of each stored tile inside its block row; tile rows g * 8 to g * 8 + 7 belong to the block row's node group g. One block holds at most 4 tiles in the rows of any one node group, and exactly 4 in the rows of its own node group (group r * 8 + c of block r, c); in every block row one node group receives exactly 4 tiles from every block of that block row. The same position may repeat, and such tiles add. `tile_cols`: tile column of each stored tile inside its block column; tiles in the rows of the block's own node group lie in that group's columns.
All inputs are finite; a program needn't handle non-finite values.
Results may differ from a plain program's by a relative error of at most 0.00044.
Values may be sent and summed in bfloat16 or wider, within the bound.
No kernel may reach another device: no remote copies, remote signals or barrier semaphores. Data moves between devices by JAX's collectives and lax.ppermute only.
A program may use at most 64 MiB of HBM per device.

v0:
```python
import jax
import jax.numpy as jnp
from jax import lax
from jax.sharding import PartitionSpec as P

CENTER = 1.0
HALF_WIDTH = 0.5


def local(tiles, tile_rows, tile_cols, start_vectors):
    tile_block = tiles[0, 0]
    row_of_tile = tile_rows[0, 0]
    col_of_tile = tile_cols[0, 0]
    tile_width = tile_block.shape[-1]
    vectors_n = start_vectors.shape[0]
    own_nodes = start_vectors.shape[1]
    rows_n = lax.axis_size("row")
    cols_n = lax.axis_size("col")
    total_nodes = own_nodes * rows_n * cols_n
    group_tiles = own_nodes // tile_width
    row_tiles = group_tiles * cols_n
    col_tiles = group_tiles * rows_n
    highest = lax.Precision.HIGHEST
    row_onehot = (row_of_tile[:, None] == jnp.arange(row_tiles, dtype=jnp.int32)[None, :]).astype(
        jnp.float32
    )
    col_onehot = (col_of_tile[:, None] == jnp.arange(col_tiles, dtype=jnp.int32)[None, :]).astype(
        jnp.float32
    )
    row_part = jnp.sum(tile_block, axis=2, dtype=jnp.float32)
    col_part = jnp.sum(tile_block, axis=1, dtype=jnp.float32)
    row_degree = jnp.dot(row_onehot.T, row_part, precision=highest).reshape(
        1, row_tiles * tile_width
    )
    col_degree = jnp.dot(col_onehot.T, col_part, precision=highest).reshape(
        1, col_tiles * tile_width
    )

    def terms(vectors):
        rounded = vectors.astype(jnp.bfloat16)
        column_panel = lax.all_gather(rounded, "row", axis=1, tiled=True)
        row_panel = lax.all_gather(rounded, "col", axis=1, tiled=True)
        picked_cols = jnp.take(
            column_panel.reshape(vectors_n, col_tiles, tile_width), col_of_tile, axis=1
        )
        picked_rows = jnp.take(
            row_panel.reshape(vectors_n, row_tiles, tile_width), row_of_tile, axis=1
        )
        row_prod = jnp.einsum(
            "tij,ktj->kti", tile_block, picked_cols, preferred_element_type=jnp.float32
        )
        col_prod = jnp.einsum(
            "tij,kti->ktj", tile_block, picked_rows, preferred_element_type=jnp.float32
        )
        col_term = jnp.einsum(
            "ktj,tq->kqj",
            col_prod,
            col_onehot,
            precision=highest,
            preferred_element_type=jnp.float32,
        )
        return (row_prod, col_term.reshape(vectors_n, col_tiles * tile_width))

    def dense_rows(row_prod):
        spread = jnp.einsum(
            "kti,tr->kri",
            row_prod,
            row_onehot,
            precision=highest,
            preferred_element_type=jnp.float32,
        )
        return spread.reshape(vectors_n, row_tiles * tile_width)

    def row_sums(row_prod):
        return lax.psum_scatter(dense_rows(row_prod), "col", scatter_dimension=1, tiled=True)

    def laplace(vectors, degree):
        row_prod, col_term = terms(vectors)
        by_rows = row_sums(row_prod)
        by_cols = lax.psum_scatter(col_term, "row", scatter_dimension=1, tiled=True)
        return degree * vectors - 0.5 * (by_rows + by_cols)

    degree_rows = lax.psum_scatter(row_degree, "col", scatter_dimension=1, tiled=True)
    degree_cols = lax.psum_scatter(col_degree, "row", scatter_dimension=1, tiled=True)
    degree = 0.5 * (degree_rows + degree_cols)
    image = laplace(start_vectors, degree)
    first_step = (image - CENTER * start_vectors) / HALF_WIDTH
    filtered = (
        2.0 * (laplace(first_step, degree) - CENTER * first_step) / HALF_WIDTH - start_vectors
    )
    gram_matrix = (
        lax.psum(jnp.dot(filtered, filtered.T, precision=highest), ("row", "col")) / total_nodes
    )
    factor = jnp.linalg.cholesky(gram_matrix)
    inverse = jax.scipy.linalg.solve_triangular(
        factor, jnp.eye(vectors_n, dtype=jnp.float32), lower=True
    )
    block = jnp.dot(inverse, filtered, precision=highest)
    image = laplace(block, degree)
    rayleigh = lax.psum(jnp.dot(block, image.T, precision=highest), ("row", "col")) / total_nodes
    ritz = jnp.dot(rayleigh.T, block, precision=highest)
    return (ritz, rayleigh)


def solution(mesh):
    placed = (
        P("row", "col", None, None, None),
        P("row", "col", None),
        P("row", "col", None),
        P(None, ("row", "col")),
    )
    return jax.shard_map(
        local, mesh=mesh, in_specs=placed, out_specs=(P(None, ("row", "col")), P()), check_vma=False
    )
```

profile of v0, /device:TPU:0, one launch (start us, length us, event | category | flops | bytes accessed | tf_op | source)
XLA Modules:
  0.0 494.9 jit_solution(11530992699287135783)
XLA Ops:
  8.0 1.6 convert_element_type.17
  9.7 1.6 convert_reduce_fusion
  11.3 0.8 fusion.54
  12.1 2.0 copy.54
  14.5 2.6 copy.52
  18.0 24.4 %all_gather.18 = bf16[64,4096]{1,0:T(8,128)(2,1)S(1)} all-gather(bf16[64,1024]{1,0:T(8,128)(2,1)S(1)} %copy-done.2), channel_id=1, replica_groups=mesh['row'=4,'col'=8] {'row'}, dimensions={1}, use_global_device_ids=true | all-gather | bytes 655360 | tf_op jit(solution)/shard_map/all_gather | solution.py:41
  43.2 0.8 convolution_bitcast_fusion.5
  44.1 1.7 fusion.16
  45.8 2.5 copy.94
  48.5 1.5 copy_bitcast_fusion.8
  51.1 1.3 fusion.14
  52.4 1.7 copy.97
  54.2 12.9 %reduce-scatter.27.cloned.1.call-done = f32[1024,1]{1,0:T(8,128)} async-done(((f32[4096,1]{1,0:T(8,128)}), f32[1024,1]{1,0:T(8,128)}) %reduce-scatter.27.cloned.1.call-update) | async-done | bytes 4112
  67.1 1.2 copy.55
  68.3 54.5 %reduce-scatter.25.cloned.1.call-done = f32[1024,1]{1,0:T(8,128)} async-done(((f32[8192,1]{1,0:T(8,128)}), f32[1024,1]{1,0:T(8,128)}) %reduce-scatter.25.cloned.1.call-update) | async-done | bytes 4112
  122.8 1.2 copy.53
  124.0 43.0 %reduce-scatter.13.cloned.1.call-done = f32[64,1024]{1,0:T(8,128)} async-done(((f32[64,8192]{1,0:T(8,128)}), f32[64,1024]{1,0:T(8,128)}) %reduce-scatter.13.cloned.1.call-update) | async-done | bytes 262160 | tf_op jit(solution)/shard_map/reduce_scatter | solution.py:75
  167.0 29.6 %reduce-scatter.15.cloned.1.call-done = f32[64,1024]{1,0:T(8,128)} async-done(((f32[64,4096]{1,0:T(8,128)}), f32[64,1024]{1,0:T(8,128)}) %reduce-scatter.15.cloned.1.call-update) | async-done | bytes 262160 | tf_op jit(solution)/shard_map/reduce_scatter | solution.py:80
  196.7 1.7 multiply_convert_fusion
  198.5 16.4 %all_gather.20 = bf16[64,4096]{1,0:T(8,128)(2,1)S(1)} all-gather(bf16[64,1024]{1,0:T(8,128)(2,1)} %multiply_convert_fusion), channel_id=1, replica_groups=mesh['row'=4,'col'=8] {'row'}, dimensions={1}, use_global_device_ids=true | all-gather | bytes 655360 | tf_op jit(solution)/shard_map/all_gather | solution.py:41
  215.7 0.8 convolution_bitcast_fusion.3
  216.5 1.7 fusion.12
  218.3 2.5 copy.93
  220.9 1.5 copy_bitcast_fusion.7
  223.5 1.3 fusion.10
  224.8 1.6 copy.96
  226.5 38.6 %reduce-scatter.17.cloned.1.call-done = f32[64,1024]{1,0:T(8,128)} async-done(((f32[64,8192]{1,0:T(8,128)}), f32[64,1024]{1,0:T(8,128)}) %reduce-scatter.17.cloned.1.call-update) | async-done | bytes 262160 | tf_op jit(solution)/shard_map/reduce_scatter | solution.py:75
  265.2 29.4 %reduce-scatter.19.cloned.1.call-done = f32[64,1024]{1,0:T(8,128)} async-done(((f32[64,4096]{1,0:T(8,128)}), f32[64,1024]{1,0:T(8,128)}) %reduce-scatter.19.cloned.1.call-update) | async-done | bytes 262160 | tf_op jit(solution)/shard_map/reduce_scatter | solution.py:80
  294.6 1.2 multiply_subtract_fusion
  296.1 39.0 %psum.14 = f32[64,64]{0,1:T(8,128)S(1)} all-reduce(f32[64,64]{0,1:T(8,128)S(1)} %fusion.80), channel_id=1, replica_groups=mesh['row'=4,'col'=8] {'row','col'}, use_global_device_ids=true, to_apply=%region_8.11 | all-reduce | flops 4096 | bytes 32768 | tf_op jit(solution)/shard_map/psum | solution.py:92
  335.3 5.8 %cholesky.17 = f32[64,64]{1,0:T(8,128)S(1)} custom-call(f32[64,64]{1,0:T(8,128)S(1)} %fusion.52), custom_call_target="Cholesky" | custom-call | tf_op jit(solution)/shard_map/jit(cholesky)/cholesky | solution.py:94
  341.8 0.7 fusion.49
  342.5 4.9 custom-call.7
  347.6 1.0 fusion.79
  348.7 16.3 %all_gather.22 = bf16[64,4096]{1,0:T(8,128)(2,1)S(1)} all-gather(bf16[64,1024]{1,0:T(8,128)(2,1)} %get-tuple-element.14), channel_id=1, replica_groups=mesh['row'=4,'col'=8] {'row'}, dimensions={1}, use_global_device_ids=true | all-gather | bytes 655360 | tf_op jit(solution)/shard_map/all_gather | solution.py:41
  365.8 0.8 convolution_bitcast_fusion.1
  366.6 1.7 fusion.8
  368.3 2.5 copy.92
  370.9 0.9 all-gather.8.cloned.1.call-done
  371.8 1.5 copy_bitcast_fusion.6
  374.5 1.3 fusion.6
  375.7 1.6 copy.95
  377.4 38.9 %reduce-scatter.21.cloned.1.call-done = f32[64,1024]{1,0:T(8,128)} async-done(((f32[64,8192]{1,0:T(8,128)}), f32[64,1024]{1,0:T(8,128)}) %reduce-scatter.21.cloned.1.call-update) | async-done | bytes 262160 | tf_op jit(solution)/shard_map/reduce_scatter | solution.py:75
  416.3 29.4 %reduce-scatter.23.cloned.1.call-done = f32[64,1024]{1,0:T(8,128)} async-done(((f32[64,4096]{1,0:T(8,128)}), f32[64,1024]{1,0:T(8,128)}) %reduce-scatter.23.cloned.1.call-update) | async-done | bytes 262160 | tf_op jit(solution)/shard_map/reduce_scatter | solution.py:80
  445.7 1.4 fusion.42
  447.1 38.9 %psum.15 = f32[64,64]{0,1:T(8,128)S(1)} all-reduce(f32[64,64]{0,1:T(8,128)S(1)} %fusion.42), channel_id=1, replica_groups=mesh['row'=4,'col'=8] {'row','col'}, use_global_device_ids=true, to_apply=%region_13.16 | all-reduce | flops 4096 | bytes 32768 | tf_op jit(solution)/shard_map/psum | solution.py:100
  486.0 1.1 fusion.78
  487.1 0.7 copy.49
  (67 shorter events, 8.9 us)
Async XLA Ops:
  8.0 40.5 %all-gather.4.cloned.1.call-start = ((), (), s32[]{:S(2)}) async-start(), calls=%async_computation.9 | async-start | bytes 1179648 | tf_op jit(solution)/shard_map/all_gather | solution.py:42
  9.7 57.4 %reduce-scatter.27.cloned.1.call-start = ((), (), s32[]{:S(2)}) async-start(), calls=%async_computation.18 | async-start | bytes 2621440
  12.1 2.1 copy-start.6
  14.1 108.6 %reduce-scatter.25.cloned.1.call-start = ((), (), s32[]{:S(2)}) async-start(), calls=%async_computation.17 | async-start | bytes 4718592
  17.1 0.7 copy-start.5
  17.1 0.9 copy-start.2
  17.2 26.1 %copy-start = (bf16[1,1,32,128,128]{4,3,2,1,0:T(8,128)(2,1)S(1)}, bf16[1,1,32,128,128]{4,3,2,1,0:T(8,128)(2,1)}, u32[]{:S(2)}) copy-start(bf16[1,1,32,128,128]{4,3,2,1,0:T(8,128)(2,1)} %param.8) | copy-start | bytes 3145732
  17.2 149.9 %reduce-scatter.13.cloned.1.call-start = ((), (), s32[]{:S(2)}) async-start(), calls=%async_computation.8 | async-start | bytes 2359296 | tf_op jit(solution)/shard_map/reduce_scatter | solution.py:75
  48.3 148.3 %reduce-scatter.15.cloned.1.call-start = ((), (), s32[]{:S(2)}) async-start(), calls=%async_computation.10 | async-start | bytes 1310720 | tf_op jit(solution)/shard_map/reduce_scatter | solution.py:80
  52.4 144.3 %copy-start.1 = (f32[64,1024]{1,0:T(8,128)S(1)}, f32[64,1024]{1,0:T(8,128)}, u32[]{:S(2)}) copy-start(f32[64,1024]{1,0:T(8,128)} %param.11) | copy-start | bytes 786436
  54.1 166.8 %all-gather.6.cloned.1.call-start = ((), (), s32[]{:S(2)}) async-start(), calls=%async_computation.12 | async-start | bytes 1179648 | tf_op jit(solution)/shard_map/all_gather | solution.py:42
  198.4 66.7 %reduce-scatter.17.cloned.1.call-start = ((), (), s32[]{:S(2)}) async-start(), calls=%async_computation.11 | async-start | bytes 2359296 | tf_op jit(solution)/shard_map/reduce_scatter | solution.py:75
  220.8 73.8 %reduce-scatter.19.cloned.1.call-start = ((), (), s32[]{:S(2)}) async-start(), calls=%async_computation.13 | async-start | bytes 1310720 | tf_op jit(solution)/shard_map/reduce_scatter | solution.py:80
  224.8 69.8 %copy-start.3 = (f32[64,1024]{1,0:T(8,128)S(1)}, f32[64,1024]{1,0:T(8,128)}, u32[]{:S(2)}) copy-start(f32[64,1024]{1,0:T(8,128)} %reduce-scatter.13.cloned.1.call-done) | copy-start | bytes 786436
  224.8 69.8 %copy-start.4 = (f32[64,1024]{1,0:T(8,128)S(1)}, f32[64,1024]{1,0:T(8,128)}, u32[]{:S(2)}) copy-start(f32[64,1024]{1,0:T(8,128)} %reduce-scatter.15.cloned.1.call-done) | copy-start | bytes 786436
  226.5 145.3 %all-gather.8.cloned.1.call-start = ((), (), s32[]{:S(2)}) async-start(), calls=%async_computation.15 | async-start | bytes 1179648 | tf_op jit(solution)/shard_map/all_gather | solution.py:42
  348.6 67.6 %reduce-scatter.21.cloned.1.call-start = ((), (), s32[]{:S(2)}) async-start(), calls=%async_computation.14 | async-start | bytes 2359296 | tf_op jit(solution)/shard_map/reduce_scatter | solution.py:75
  370.9 74.8 %reduce-scatter.23.cloned.1.call-start = ((), (), s32[]{:S(2)}) async-start(), calls=%async_computation.16 | async-start | bytes 1310720 | tf_op jit(solution)/shard_map/reduce_scatter | solution.py:80
Sparse Core Ops, SparseCore 0:
  11.3 26.1 all-gather.3
  198.6 22.0 all-gather.5
  223.9 41.2 reduce-scatter.16
  267.4 27.1 reduce-scatter.18
Sparse Core Ops, SparseCore 1:
  14.2 52.8 reduce-scatter.26
  70.7 52.0 reduce-scatter.24
  125.9 41.1 reduce-scatter.12
  169.5 27.1 reduce-scatter.14
  348.7 23.1 all-gather.7
  375.1 41.1 reduce-scatter.20
  418.5 27.1 reduce-scatter.22
where the time goes:
time: 496 us; the launch traced here: 495 us
  waiting for transfers between devices  278 us (56%)
  blocking collectives  135 us (27%)
  local copies, waits for them, and re-layouts  30 us (6%)
  other arithmetic  18.3 us (4%)
  matrix products  18 us (4%)
  between operations  15.7 us (3%)
    reduce_scatter x3, waiting for transfers between devices, row_sums(): lax.psum_scatter(dense_rows(row_prod), 'col', scatter_dimension=1, tiled=...  121 us
    reduce_scatter x3, waiting for transfers between devices, laplace(): by_cols = lax.psum_scatter(col_term, 'row', scatter_dimension=1, tiled=True)  88.5 us
    unnamed x13, waiting for transfers between devices  67.5 us
    all_gather x3, blocking collectives, terms(): column_panel = lax.all_gather(rounded, 'row', axis=1, tiled=True)  57 us
    psum x1, blocking collectives, local(): lax.psum(jnp.dot(filtered, filtered.T, precision=highest), ('row', 'col'))  39 us
    psum x1, blocking collectives, local(): lax.psum(jnp.dot(block, image.T, precision=highest), ('row', 'col'))  38.9 us
    unnamed x25, local copies, waits for them, and re-layouts  21.1 us
  transfers between devices with their start and end apart: 11, of which 9 were waited for; matrix products, arithmetic and copies ran while one was open for 9% of the time, Pallas kernels for 0%

commit v1 on v0

v1 whole, which is shorter than its diff:
```python
import functools

import jax
import jax.numpy as jnp
from jax import lax
from jax.experimental import pallas as pl
from jax.experimental.pallas import tpu as pltpu
from jax.sharding import PartitionSpec as P

CENTER = 1.0
HALF_WIDTH = 0.5
HIGHEST = lax.Precision.HIGHEST
NT = (((1,), (1,)), ((), ()))
NN = (((1,), (0,)), ((), ()))
BF16 = jnp.bfloat16
F32 = jnp.float32
VMEM = pl.BlockSpec(memory_space=pltpu.VMEM)
SMEM = pl.BlockSpec(memory_space=pltpu.SMEM)
DEGREE_ROWS = 16


def call(kernel, out_shape, scratch, limit, args, flops=0, smem=0):
    moved = sum(x.size * x.dtype.itemsize for x in args)
    return pl.pallas_call(
        kernel,
        out_shape=out_shape,
        in_specs=[SMEM] * smem + [VMEM] * (len(args) - smem),
        out_specs=jax.tree.map(lambda _: VMEM, out_shape),
        scratch_shapes=scratch,
        compiler_params=pltpu.CompilerParams(vmem_limit_bytes=limit * 2**20),
        cost_estimate=pl.CostEstimate(flops=flops, bytes_accessed=moved, transcendentals=0),
    )(*args)


def exchange(parts, axis):
    n = lax.axis_size(axis)
    return [
        lax.ppermute(part, axis, [(i, i ^ d) for i in range(n)])
        for d, part in zip(range(1, n), parts)
    ]


def tiles_first(ref, width):
    return [ref[:, k * width : (k + 1) * width] for k in range(ref.shape[1] // width)]


def round_kernel(vec_ref, out_ref):
    for k, piece in enumerate(tiles_first(vec_ref, out_ref.shape[2])):
        out_ref[k] = piece.astype(BF16)


def product_kernel(parts_n, degree, dims, meta, in_rows, out_rows, tiles_ref, *refs):
    part_refs, refs = refs[:parts_n], refs[parts_n:]
    own_ref, send_refs, (panel, total) = refs[0], refs[1:-2], refs[-2:]
    group, vectors_n, width = part_refs[0].shape
    me_in, me_out = meta[0], meta[1]
    for d, part in enumerate(part_refs):
        panel[d * group : (d + 1) * group, :vectors_n, :] = part[...]
    if degree:
        panel[:, vectors_n:, :] = jnp.ones(
            (panel.shape[0], panel.shape[1] - vectors_n, width), BF16
        )
    total[...] = jnp.zeros_like(total)
    for t in range(tiles_ref.shape[0]):
        source, target = in_rows[t], out_rows[t]
        source = ((source // group) ^ me_in) * group + source % group
        target = ((target // group) ^ me_out) * group + target % group
        total[target] += lax.dot_general(
            panel[source], tiles_ref[t], dims, preferred_element_type=F32
        )
    own_ref[...] = total[:group]
    for d, send in enumerate(send_refs, 1):
        send[:group] = total[d * group : (d + 1) * group, :vectors_n, :].astype(BF16)
        if degree:
            sums = jnp.concatenate(
                [total[d * group + k, vectors_n : vectors_n + 1, :] for k in range(group)], 0
            )
            high = sums.astype(BF16).astype(F32)
            low = (sums - high).astype(BF16).astype(F32)
            rest = sums - high - low
            pad = jnp.zeros((vectors_n - 3 * group, width), F32)
            send[group] = jnp.concatenate([high, low, rest, pad], 0).astype(BF16)


def products(tiles, in_rows, out_rows, meta, parts, out_n, dims, degree):
    group, vectors_n, width = parts[0].shape
    height = vectors_n + (DEGREE_ROWS if degree else 0)
    blocks = group + (1 if degree else 0)
    out_shape = [jax.ShapeDtypeStruct((group, height, width), F32)]
    out_shape += [jax.ShapeDtypeStruct((blocks, vectors_n, width), BF16)] * (out_n - 1)
    scratch = [
        pltpu.VMEM((len(parts) * group, height, width), BF16),
        pltpu.VMEM((out_n * group, height, width), F32),
    ]
    kernel = functools.partial(product_kernel, len(parts), degree, dims)
    flops = 2 * tiles.size * height
    args = [meta, in_rows, out_rows, tiles, *parts]
    own, *send = call(kernel, out_shape, scratch, 24, args, flops, 3)
    return own, send


def gathered_sum(own, received, k, rows):
    total = own[k, rows, :]
    for part in received:
        total = total + part[k, rows, :].astype(F32)
    return total


def first_kernel(rows_n, cols_n, vec_ref, row_own, col_own, *refs):
    row_refs, refs = refs[: cols_n - 1], refs[cols_n - 1 :]
    col_refs, refs = refs[: rows_n - 1], refs[rows_n - 1 :]
    first_ref, rounded_ref, degree_ref = refs
    group, vectors_n, width = rounded_ref.shape
    degree = jnp.zeros((group, width), F32)
    for own, received in ((row_own, row_refs), (col_own, col_refs)):
        degree += jnp.concatenate(
            [own[k, vectors_n : vectors_n + 1, :] for k in range(group)], 0
        )
        for part in received:
            block = part[group].astype(F32)
            degree += (block[2 * group : 3 * group] + block[group : 2 * group]) + block[:group]
    degree = 0.5 * degree
    degree_ref[...] = degree
    every = slice(0, vectors_n)
    for k, vec in enumerate(tiles_first(vec_ref, width)):
        symmetric = 0.5 * (
            gathered_sum(row_own, row_refs, k, every) + gathered_sum(col_own, col_refs, k, every)
        )
        image = degree[k : k + 1, :] * vec - symmetric
        first = (image - CENTER * vec) / HALF_WIDTH
        first_ref[:, k * width : (k + 1) * width] = first
        rounded_ref[k] = first.astype(BF16)


def filter_kernel(rows_n, cols_n, start_ref, first_ref, degree_ref, row_own, col_own, *refs):
    row_refs, refs = refs[: cols_n - 1], refs[cols_n - 1 :]
    col_refs, refs = refs[: rows_n - 1], refs[rows_n - 1 :]
    filtered_ref, rounded_ref, gram_ref, both = refs
    group, vectors_n, width = rounded_ref.shape
    every = slice(0, vectors_n)
    for k, vec in enumerate(tiles_first(first_ref, width)):
        symmetric = 0.5 * (
            gathered_sum(row_own, row_refs, k, every) + gathered_sum(col_own, col_refs, k, every)
        )
        columns = slice(k * width, (k + 1) * width)
        image = degree_ref[k : k + 1, :] * vec - symmetric
        filtered = 2.0 * (image - CENTER * vec) / HALF_WIDTH - start_ref[:, columns]
        filtered_ref[:, columns] = filtered
        rounded_ref[k] = filtered.astype(BF16)
        both[:vectors_n, columns] = filtered
        both[vectors_n:, columns] = degree_ref[k : k + 1, :] * filtered
    gram_ref[...] = lax.dot_general(
        filtered_ref[...], both[...], NT, precision=HIGHEST, preferred_element_type=F32
    )


def form_kernel(cols_n, rows_n, meta, tile_rows, tile_cols, tiles_ref, *refs):
    row_refs, refs = refs[:cols_n], refs[cols_n:]
    col_refs, refs = refs[:rows_n], refs[rows_n:]
    out_ref, row_panel, col_panel, total = refs
    group, vectors_n, width = row_refs[0].shape
    for d, part in enumerate(row_refs):
        row_panel[d * group : (d + 1) * group] = part[...]
    for d, part in enumerate(col_refs):
        col_panel[d * group : (d + 1) * group] = part[...]
    total[...] = jnp.zeros_like(total)
    for t in range(tiles_ref.shape[0]):
        row, col = tile_rows[t], tile_cols[t]
        row = ((row // group) ^ meta[1]) * group + row % group
        col = ((col // group) ^ meta[0]) * group + col % group
        product = lax.dot_general(
            col_panel[col], tiles_ref[t], NT, preferred_element_type=F32
        )
        total[...] += lax.dot_general(
            row_panel[row], product.astype(BF16), NT, preferred_element_type=F32
        )
    out_ref[...] = total[...]


def tree_sum(parts):
    while len(parts) > 1:
        parts = [a + b for a, b in zip(parts[::2], parts[1::2])]
    return parts[0]


def all_sum(part):
    for axis in ("col", "row"):
        n = lax.axis_size(axis)
        part = tree_sum([part, *exchange([part] * (n - 1), axis)])
    return part


def local(tiles, tile_rows, tile_cols, start):
    tiles, tile_rows, tile_cols = tiles[0, 0], tile_rows[0, 0], tile_cols[0, 0]
    width = tiles.shape[-1]
    vectors_n, own_nodes = start.shape
    rows_n, cols_n = lax.axis_size("row"), lax.axis_size("col")
    total_nodes = own_nodes * rows_n * cols_n
    group = own_nodes // width
    row_me, col_me = lax.axis_index("row"), lax.axis_index("col")
    meta = jnp.stack([row_me, col_me]).astype(jnp.int32)
    swapped = jnp.stack([col_me, row_me]).astype(jnp.int32)

    rounded_shape = jax.ShapeDtypeStruct((group, vectors_n, width), BF16)
    vector_shape = jax.ShapeDtypeStruct((vectors_n, own_nodes), F32)

    def gather(rounded):
        col_parts = [rounded, *exchange([rounded] * (rows_n - 1), "row")]
        row_parts = [rounded, *exchange([rounded] * (cols_n - 1), "col")]
        return col_parts, row_parts

    def apply(rounded, degree):
        col_parts, row_parts = gather(rounded)
        col_own, col_send = products(
            tiles, tile_rows, tile_cols, swapped, row_parts, rows_n, NN, degree
        )
        col_got = exchange(col_send, "row")
        row_own, row_send = products(
            tiles, tile_cols, tile_rows, meta, col_parts, cols_n, NT, degree
        )
        row_got = exchange(row_send, "col")
        return [row_own, col_own, *row_got, *col_got]

    rounded = call(round_kernel, rounded_shape, [], 16, [start])
    sums = apply(rounded, True)
    first, rounded, degree = call(
        functools.partial(first_kernel, rows_n, cols_n),
        [vector_shape, rounded_shape, jax.ShapeDtypeStruct((group, width), F32)],
        [],
        24,
        [start, *sums],
    )
    sums = apply(rounded, False)
    filtered, rounded, gram = call(
        functools.partial(filter_kernel, rows_n, cols_n),
        [vector_shape, rounded_shape, jax.ShapeDtypeStruct((vectors_n, 2 * vectors_n), F32)],
        [pltpu.VMEM((2 * vectors_n, own_nodes), F32)],
        24,
        [start, first, degree, *sums],
    )
    col_parts, row_parts = gather(rounded)
    gram = all_sum(gram) / total_nodes
    factor = jnp.linalg.cholesky(gram[:, :vectors_n])
    inverse = jax.scipy.linalg.solve_triangular(
        factor, jnp.eye(vectors_n, dtype=F32), lower=True
    )
    form = call(
        functools.partial(form_kernel, cols_n, rows_n),
        jax.ShapeDtypeStruct((vectors_n, vectors_n), F32),
        [
            pltpu.VMEM((cols_n * group, vectors_n, width), BF16),
            pltpu.VMEM((rows_n * group, vectors_n, width), BF16),
            pltpu.VMEM((vectors_n, vectors_n), F32),
        ],
        24,
        [meta, tile_rows, tile_cols, tiles, *row_parts, *col_parts],
        2 * tiles.size * vectors_n,
        3,
    )
    form = all_sum(form) / total_nodes
    projected = gram[:, vectors_n:] - 0.5 * (form + form.T)
    rayleigh = jnp.dot(
        jnp.dot(inverse, projected, precision=HIGHEST), inverse.T, precision=HIGHEST
    )
    ritz = jnp.dot(
        jnp.dot(rayleigh.T, inverse, precision=HIGHEST), filtered, precision=HIGHEST
    )
    return (ritz, rayleigh)


def solution(mesh):
    placed = (
        P("row", "col", None, None, None),
        P("row", "col", None),
        P("row", "col", None),
        P(None, ("row", "col")),
    )
    return jax.shard_map(
        local, mesh=mesh, in_specs=placed, out_specs=(P(None, ("row", "col")), P()), check_vma=False
    )
```

time: 496 us -> 170 us (0.34)
  waiting for transfers between devices: 278 us -> 52.2 us
  blocking collectives: 135 us -> 0 us
  starting transfers between devices: 0.47 us -> 85.8 us
  local copies, waits for them, and re-layouts: 30 us -> 3.35 us
  matrix products: 18 us -> 1.93 us
  between operations: 15.7 us -> 0.94 us
  Pallas kernels: 0 us -> 12.9 us
  other arithmetic: 18.3 us -> 12.3 us
    reduce_scatter x6 -> x0, waiting for transfers between devices: 209 us -> none  [the longest x3 121 us: row_sums(): lax.psum_scatter(dense_rows(row_prod), 'col', scatter_dimension=1, tiled=...]
    ppermute x0 -> x70, starting transfers between devices: none -> 85.8 us  [exchange(): lax.ppermute(part, axis, [(i, i ^ d) for i in range(n)])]
    psum x2 -> x0, blocking collectives: 77.9 us -> none  [the longest x1 39 us: local(): lax.psum(jnp.dot(filtered, filtered.T, precision=highest), ('row', 'col'))]
    unnamed x13 -> x0, waiting for transfers between devices: 67.5 us -> none
    all_gather x3 -> x0, blocking collectives: 57 us -> none  [terms(): column_panel = lax.all_gather(rounded, 'row', axis=1, tiled=True)]
    ppermute x0 -> x70, waiting for transfers between devices: none -> 52.2 us  [exchange(): lax.ppermute(part, axis, [(i, i ^ d) for i in range(n)])]
    unnamed x25 -> x14, local copies, waits for them, and re-layouts: 21.1 us -> 3.21 us
    dot_general x18 -> x4, matrix products: 17.8 us -> 1.72 us  [the longest x1 1.06 us: local(): jnp.dot(jnp.dot(rayleigh.T, inverse, precision=HIGHEST), filtered, precis...]
  transfers between devices with their start and end apart: 11 -> 70, of which waited for: 9 -> 25; matrix products, arithmetic and copies ran while one was open for 9% -> 7% of each run, Pallas kernels for 0% -> 3%
where the time goes in v1:
time: 170 us; the launch traced here: 169 us
  starting transfers between devices  85.8 us (50%)
  waiting for transfers between devices  52.2 us (31%)
  Pallas kernels  12.9 us (8%)
  other arithmetic  12.3 us (7%)
  local copies, waits for them, and re-layouts  3.35 us (2%)
  matrix products  1.93 us (1%)
    ppermute x70, starting transfers between devices, exchange(): lax.ppermute(part, axis, [(i, i ^ d) for i in range(n)])  85.8 us
    ppermute x70, waiting for transfers between devices, exchange(): lax.ppermute(part, axis, [(i, i ^ d) for i in range(n)])  52.2 us
    pallas_call x8, Pallas kernels, call(): pl.pallas_call(kernel, out_shape=out_shape, in_specs=[SMEM] * smem + [VME...  12.9 us
    another operation x3, other arithmetic, local(): factor = jnp.linalg.cholesky(gram[:, :vectors_n])  6.51 us
    another operation x2, other arithmetic, local(): jax.scipy.linalg.solve_triangular(factor, jnp.eye(vectors_n, dtype=F32),...  5.55 us
  transfers between devices with their start and end apart: 70, of which 25 were waited for; matrix products, arithmetic and copies ran while one was open for 7% of the time, Pallas kernels for 3%

profile of v1, /device:TPU:0, one launch (start us, length us, event | category | flops | bytes accessed | tf_op | source)
XLA Modules:
  0.0 169.3 jit_solution(10075131051279230494)
XLA Ops:
  1.6 3.4 %collective-permute-start.9 = (bf16[8,64,128]{2,1,0:T(8,128)(2,1)S(1)}, bf16[8,64,128]{2,1,0:T(8,128)(2,1)S(1)}, u32[]{:S(2)}, u32[]{:S(2)}) collective-permute-start(bf16[8,64,128]{2,1,0:T(8,128)(2,1)S(1)} %shard_map.59.refs_0_), channel_id=1, source_target_pairs={{0,7},{1,6},{2,5},{3,4},{4,3},{5,2},{6,1},{7,0},{8,15},{9,14},{10,... | collective-permute-start | bytes 393224 | tf_op jit(solution)/shard_map/ppermute | solution.py:38
  5.6 1.4 collective-permute-start.7
  8.9 2.5 %collective-permute-start.4 = (bf16[8,64,128]{2,1,0:T(8,128)(2,1)S(1)}, bf16[8,64,128]{2,1,0:T(8,128)(2,1)S(1)}, u32[]{:S(2)}, u32[]{:S(2)}) collective-permute-start(bf16[8,64,128]{2,1,0:T(8,128)(2,1)S(1)} %shard_map.59.refs_0_), channel_id=1, source_target_pairs={{0,2},{1,3},{2,0},{3,1},{4,6},{5,7},{6,4},{7,5},{8,10},{9,11},{10,... | collective-permute-start | bytes 393224 | tf_op jit(solution)/shard_map/ppermute | solution.py:38
  12.3 2.4 %collective-permute-done.7.refs_5_ = bf16[8,64,128]{2,1,0:T(8,128)(2,1)S(1)} collective-permute-done((bf16[8,64,128]{2,1,0:T(8,128)(2,1)S(1)}, bf16[8,64,128]{2,1,0:T(8,128)(2,1)S(1)}, u32[]{:S(2)}, u32[]{:S(2)}) %collective-permute-start.7) | collective-permute-done | bytes 131104 | tf_op jit(solution)/shard_map/ppermute | solution.py:38
  14.7 4.3 %collective-permute-start.2 = (bf16[8,64,128]{2,1,0:T(8,128)(2,1)S(1)}, bf16[8,64,128]{2,1,0:T(8,128)(2,1)S(1)}, u32[]{:S(2)}, u32[]{:S(2)}) collective-permute-start(bf16[8,64,128]{2,1,0:T(8,128)(2,1)S(1)} %shard_map.59.refs_0_), channel_id=1, source_target_pairs={{0,24},{8,16},{16,8},{24,0},{1,25},{9,17},{17,9},{25,1},{2,26},{10... | collective-permute-start | bytes 393224 | tf_op jit(solution)/shard_map/ppermute | solution.py:38
  19.0 1.8 %collective-permute-start.1 = (bf16[8,64,128]{2,1,0:T(8,128)(2,1)S(1)}, bf16[8,64,128]{2,1,0:T(8,128)(2,1)S(1)}, u32[]{:S(2)}, u32[]{:S(2)}) collective-permute-start(bf16[8,64,128]{2,1,0:T(8,128)(2,1)S(1)} %shard_map.59.refs_0_), channel_id=1, source_target_pairs={{0,16},{8,24},{16,0},{24,8},{1,17},{9,25},{17,1},{25,9},{2,18},{10... | collective-permute-start | bytes 393224 | tf_op jit(solution)/shard_map/ppermute | solution.py:38
  20.8 1.6 collective-permute-start
  27.5 2.8 %collective-permute-start.19 = (bf16[9,64,128]{2,1,0:T(8,128)(2,1)S(1)}, bf16[9,64,128]{2,1,0:T(8,128)(2,1)S(1)}, u32[]{:S(2)}, u32[]{:S(2)}) collective-permute-start(bf16[9,64,128]{2,1,0:T(8,128)(2,1)S(1)} %get-tuple-element.43), channel_id=1, source_target_pairs={{0,24},{8,16},{16,8},{24,0},{1,25},{9,17},{17,9},{25,1},{2,26},{10... | collective-permute-start | bytes 442376 | tf_op jit(solution)/shard_map/ppermute | solution.py:38
  31.6 1.7 %shard_map.60 = (f32[8,80,128]{2,1,0:T(8,128)S(1)}, bf16[9,64,128]{2,1,0:T(8,128)(2,1)S(1)}, bf16[9,64,128]{2,1,0:T(8,128)(2,1)S(1)}, bf16[9,64,128]{2,1,0:T(8,1...) custom-call(s32[2]{0:T(128)S(1)} %pad_add_fusion.meta, ...), custom_call_target="tpu_custom_call" | custom-call | flops 83886080 | bytes 1573128 | tf_op jit(solution)/shard_map/pallas_call | solution.py:24
  33.4 1.5 collective-permute-start.11
  36.0 4.7 %collective-permute-done.18.refs_8_ = bf16[9,64,128]{2,1,0:T(8,128)(2,1)S(1)} collective-permute-done((bf16[9,64,128]{2,1,0:T(8,128)(2,1)S(1)}, bf16[9,64,128]{2,1,0:T(8,128)(2,1)S(1)}, u32[]{:S(2)}, u32[]{:S(2)}) %collective-permute-start.18) | collective-permute-done | bytes 147488 | tf_op jit(solution)/shard_map/ppermute | solution.py:38
  40.7 1.5 collective-permute-start.13
  42.2 1.5 collective-permute-start.15
  43.7 1.4 collective-permute-start.16
  45.1 7.7 %collective-permute-done.13.refs_3_ = bf16[9,64,128]{2,1,0:T(8,128)(2,1)S(1)} collective-permute-done((bf16[9,64,128]{2,1,0:T(8,128)(2,1)S(1)}, bf16[9,64,128]{2,1,0:T(8,128)(2,1)S(1)}, u32[]{:S(2)}, u32[]{:S(2)}) %collective-permute-start.13) | collective-permute-done | bytes 147488 | tf_op jit(solution)/shard_map/ppermute | solution.py:38
  52.8 1.8 %collective-permute-done.14.refs_4_ = bf16[9,64,128]{2,1,0:T(8,128)(2,1)S(1)} collective-permute-done((bf16[9,64,128]{2,1,0:T(8,128)(2,1)S(1)}, bf16[9,64,128]{2,1,0:T(8,128)(2,1)S(1)}, u32[]{:S(2)}, u32[]{:S(2)}) %collective-permute-start.14) | collective-permute-done | bytes 147488 | tf_op jit(solution)/shard_map/ppermute | solution.py:38
  54.9 2.5 %collective-permute-start.29 = (bf16[8,64,128]{2,1,0:T(8,128)(2,1)S(1)}, bf16[8,64,128]{2,1,0:T(8,128)(2,1)S(1)}, u32[]{:S(2)}, u32[]{:S(2)}) collective-permute-start(bf16[8,64,128]{2,1,0:T(8,128)(2,1)S(1)} %get-tuple-element.46.refs_0_), channel_id=1, source_target_pairs={{0,7},{1,6},{2,5},{3,4},{4,3},{5,2},{6,1},{7,0},{8,15},{9,14},{10,... | collective-permute-start | bytes 393224 | tf_op jit(solution)/shard_map/ppermute | solution.py:38
  58.0 1.5 collective-permute-start.26
  59.5 1.4 collective-permute-start.25
  62.6 2.6 %collective-permute-done.28.refs_6_ = bf16[8,64,128]{2,1,0:T(8,128)(2,1)S(1)} collective-permute-done((bf16[8,64,128]{2,1,0:T(8,128)(2,1)S(1)}, bf16[8,64,128]{2,1,0:T(8,128)(2,1)S(1)}, u32[]{:S(2)}, u32[]{:S(2)}) %collective-permute-start.28) | collective-permute-done | bytes 131104 | tf_op jit(solution)/shard_map/ppermute | solution.py:38
  65.1 2.1 %collective-permute-done.27.refs_5_ = bf16[8,64,128]{2,1,0:T(8,128)(2,1)S(1)} collective-permute-done((bf16[8,64,128]{2,1,0:T(8,128)(2,1)S(1)}, bf16[8,64,128]{2,1,0:T(8,128)(2,1)S(1)}, u32[]{:S(2)}, u32[]{:S(2)}) %collective-permute-start.27) | collective-permute-done | bytes 131104 | tf_op jit(solution)/shard_map/ppermute | solution.py:38
  67.3 2.5 %collective-permute-start.22 = (bf16[8,64,128]{2,1,0:T(8,128)(2,1)S(1)}, bf16[8,64,128]{2,1,0:T(8,128)(2,1)S(1)}, u32[]{:S(2)}, u32[]{:S(2)}) collective-permute-start(bf16[8,64,128]{2,1,0:T(8,128)(2,1)S(1)} %get-tuple-element.46.refs_0_), channel_id=1, source_target_pairs={{0,24},{8,16},{16,8},{24,0},{1,25},{9,17},{17,9},{25,1},{2,26},{10... | collective-permute-start | bytes 393224 | tf_op jit(solution)/shard_map/ppermute | solution.py:38
  70.1 2.4 %collective-permute-start.21 = (bf16[8,64,128]{2,1,0:T(8,128)(2,1)S(1)}, bf16[8,64,128]{2,1,0:T(8,128)(2,1)S(1)}, u32[]{:S(2)}, u32[]{:S(2)}) collective-permute-start(bf16[8,64,128]{2,1,0:T(8,128)(2,1)S(1)} %get-tuple-element.46.refs_0_), channel_id=1, source_target_pairs={{0,16},{8,24},{16,0},{24,8},{1,17},{9,25},{17,1},{25,9},{2,18},{10... | collective-permute-start | bytes 393224 | tf_op jit(solution)/shard_map/ppermute | solution.py:38
  74.3 1.5 collective-permute-start.37
  76.3 2.5 %collective-permute-start.39 = (bf16[8,64,128]{2,1,0:T(8,128)(2,1)S(1)}, bf16[8,64,128]{2,1,0:T(8,128)(2,1)S(1)}, u32[]{:S(2)}, u32[]{:S(2)}) collective-permute-start(bf16[8,64,128]{2,1,0:T(8,128)(2,1)S(1)} %get-tuple-element.58), channel_id=1, source_target_pairs={{0,24},{8,16},{16,8},{24,0},{1,25},{9,17},{17,9},{25,1},{2,26},{10... | collective-permute-start | bytes 393224 | tf_op jit(solution)/shard_map/ppermute | solution.py:38
  78.8 4.7 %collective-permute-done.21.refs_2_ = bf16[8,64,128]{2,1,0:T(8,128)(2,1)S(1)} collective-permute-done((bf16[8,64,128]{2,1,0:T(8,128)(2,1)S(1)}, bf16[8,64,128]{2,1,0:T(8,128)(2,1)S(1)}, u32[]{:S(2)}, u32[]{:S(2)}) %collective-permute-start.21) | collective-permute-done | bytes 131104 | tf_op jit(solution)/shard_map/ppermute | solution.py:38
  83.5 1.4 shard_map.63
  85.0 1.7 collective-permute-start.31
  86.8 4.5 %collective-permute-done.38.refs_8_ = bf16[8,64,128]{2,1,0:T(8,128)(2,1)S(1)} collective-permute-done((bf16[8,64,128]{2,1,0:T(8,128)(2,1)S(1)}, bf16[8,64,128]{2,1,0:T(8,128)(2,1)S(1)}, u32[]{:S(2)}, u32[]{:S(2)}) %collective-permute-start.38) | collective-permute-done | bytes 131104 | tf_op jit(solution)/shard_map/ppermute | solution.py:38
  92.2 2.2 %collective-permute-start.35 = (bf16[8,64,128]{2,1,0:T(8,128)(2,1)S(1)}, bf16[8,64,128]{2,1,0:T(8,128)(2,1)S(1)}, u32[]{:S(2)}, u32[]{:S(2)}) collective-permute-start(bf16[8,64,128]{2,1,0:T(8,128)(2,1)S(1)} %get-tuple-element.54), channel_id=1, source_target_pairs={{0,6},{1,7},{2,4},{3,5},{4,2},{5,3},{6,0},{7,1},{8,14},{9,15},{10,... | collective-permute-start | bytes 393224 | tf_op jit(solution)/shard_map/ppermute | solution.py:38
  95.7 7.3 %collective-permute-done.33.refs_3_ = bf16[8,64,128]{2,1,0:T(8,128)(2,1)S(1)} collective-permute-done((bf16[8,64,128]{2,1,0:T(8,128)(2,1)S(1)}, bf16[8,64,128]{2,1,0:T(8,128)(2,1)S(1)}, u32[]{:S(2)}, u32[]{:S(2)}) %collective-permute-start.33) | collective-permute-done | bytes 131104 | tf_op jit(solution)/shard_map/ppermute | solution.py:38
  104.5 2.3 %collective-permute-start.46 = (f32[64,128]{1,0:T(8,128)S(1)}, f32[64,128]{1,0:T(8,128)S(1)}, u32[]{:S(2)}, u32[]{:S(2)}) collective-permute-start(f32[64,128]{1,0:T(8,128)S(1)} %get-tuple-element.59), channel_id=1, source_target_pairs={{0,7},{1,6},{2,5},{3,4},{4,3},{5,2},{6,1},{7,0},{8,15},{9,14},{10,... | collective-permute-start | bytes 98312 | tf_op jit(solution)/shard_map/ppermute | solution.py:38
  108.9 2.1 %collective-permute-start.42 = (f32[64,128]{1,0:T(8,128)S(1)}, f32[64,128]{1,0:T(8,128)S(1)}, u32[]{:S(2)}, u32[]{:S(2)}) collective-permute-start(f32[64,128]{1,0:T(8,128)S(1)} %get-tuple-element.59), channel_id=1, source_target_pairs={{0,3},{1,2},{2,1},{3,0},{4,7},{5,6},{6,5},{7,4},{8,11},{9,10},{10,... | collective-permute-start | bytes 98312 | tf_op jit(solution)/shard_map/ppermute | solution.py:38
  112.6 2.3 %collective-permute-done.41 = f32[64,128]{1,0:T(8,128)S(1)} collective-permute-done((f32[64,128]{1,0:T(8,128)S(1)}, f32[64,128]{1,0:T(8,128)S(1)}, u32[]{:S(2)}, u32[]{:S(2)}) %collective-permute-start.41) | collective-permute-done | bytes 32800 | tf_op jit(solution)/shard_map/ppermute | solution.py:38
  114.9 2.5 %collective-permute-start.49 = (f32[64,128]{1,0:T(8,128)S(1)}, f32[64,128]{1,0:T(8,128)S(1)}, u32[]{:S(2)}, u32[]{:S(2)}) collective-permute-start(f32[64,128]{1,0:T(8,128)S(1)} %add_add_fusion.1), channel_id=1, source_target_pairs={{0,24},{8,16},{16,8},{24,0},{1,25},{9,17},{17,9},{25,1},{2,26},{10... | collective-permute-start | bytes 98312 | tf_op jit(solution)/shard_map/ppermute | solution.py:38
  117.5 1.9 %collective-permute-start.47 = (f32[64,128]{1,0:T(8,128)S(1)}, f32[64,128]{1,0:T(8,128)S(1)}, u32[]{:S(2)}, u32[]{:S(2)}) collective-permute-start(f32[64,128]{1,0:T(8,128)S(1)} %add_add_fusion.1), channel_id=1, source_target_pairs={{0,8},{8,0},{16,24},{24,16},{1,9},{9,1},{17,25},{25,17},{2,10},{10... | collective-permute-start | bytes 98312 | tf_op jit(solution)/shard_map/ppermute | solution.py:38
  119.4 2.5 %collective-permute-start.59 = (bf16[8,64,128]{2,1,0:T(8,128)(2,1)S(1)}, bf16[8,64,128]{2,1,0:T(8,128)(2,1)S(1)}, u32[]{:S(2)}, u32[]{:S(2)}) collective-permute-start(bf16[8,64,128]{2,1,0:T(8,128)(2,1)S(1)} %get-tuple-element.60.refs_0_.refs_8_), channel_id=1, source_target_pairs={{0,24},{8,16},{16,8},{24,0},{1,25},{9,17},{17,9},{25,1},{2,26},{10... | collective-permute-start | bytes 393224 | tf_op jit(solution)/shard_map/ppermute | solution.py:38
  121.9 1.9 %collective-permute-start.57 = (bf16[8,64,128]{2,1,0:T(8,128)(2,1)S(1)}, bf16[8,64,128]{2,1,0:T(8,128)(2,1)S(1)}, u32[]{:S(2)}, u32[]{:S(2)}) collective-permute-start(bf16[8,64,128]{2,1,0:T(8,128)(2,1)S(1)} %get-tuple-element.60.refs_0_.refs_8_), channel_id=1, source_target_pairs={{0,8},{8,0},{16,24},{24,16},{1,9},{9,1},{17,25},{25,17},{2,10},{10... | collective-permute-start | bytes 393224 | tf_op jit(solution)/shard_map/ppermute | solution.py:38
  123.8 1.8 %collective-permute-done.48 = f32[64,128]{1,0:T(8,128)S(1)} collective-permute-done((f32[64,128]{1,0:T(8,128)S(1)}, f32[64,128]{1,0:T(8,128)S(1)}, u32[]{:S(2)}, u32[]{:S(2)}) %collective-permute-start.48) | collective-permute-done | bytes 32800 | tf_op jit(solution)/shard_map/ppermute | solution.py:38
  125.6 2.0 %collective-permute-start.55 = (bf16[8,64,128]{2,1,0:T(8,128)(2,1)S(1)}, bf16[8,64,128]{2,1,0:T(8,128)(2,1)S(1)}, u32[]{:S(2)}, u32[]{:S(2)}) collective-permute-start(bf16[8,64,128]{2,1,0:T(8,128)(2,1)S(1)} %get-tuple-element.60.refs_0_.refs_8_), channel_id=1, source_target_pairs={{0,6},{1,7},{2,4},{3,5},{4,2},{5,3},{6,0},{7,1},{8,14},{9,15},{10,... | collective-permute-start | bytes 393224 | tf_op jit(solution)/shard_map/ppermute | solution.py:38
  127.7 2.4 %collective-permute-start.54 = (bf16[8,64,128]{2,1,0:T(8,128)(2,1)S(1)}, bf16[8,64,128]{2,1,0:T(8,128)(2,1)S(1)}, u32[]{:S(2)}, u32[]{:S(2)}) collective-permute-start(bf16[8,64,128]{2,1,0:T(8,128)(2,1)S(1)} %get-tuple-element.60.refs_0_.refs_8_), channel_id=1, source_target_pairs={{0,5},{1,4},{2,7},{3,6},{4,1},{5,0},{6,3},{7,2},{8,13},{9,12},{10,... | collective-permute-start | bytes 393224 | tf_op jit(solution)/shard_map/ppermute | solution.py:38
  130.1 2.2 %collective-permute-done.58.refs_10_ = bf16[8,64,128]{2,1,0:T(8,128)(2,1)S(1)} collective-permute-done((bf16[8,64,128]{2,1,0:T(8,128)(2,1)S(1)}, bf16[8,64,128]{2,1,0:T(8,128)(2,1)S(1)}, u32[]{:S(2)}, u32[]{:S(2)}) %collective-permute-start.58) | collective-permute-done | bytes 131104 | tf_op jit(solution)/shard_map/ppermute | solution.py:38
  135.3 5.8 %cholesky.17 = f32[64,64]{1,0:T(8,128)S(1)} custom-call(f32[64,64]{1,0:T(8,128)S(1)} %fusion.6), custom_call_target="Cholesky" | custom-call | tf_op jit(solution)/shard_map/jit(cholesky)/cholesky | solution.py:243
  141.2 6.0 %shard_map.66 = f32[64,64]{1,0:T(8,128)S(1)} custom-call(s32[2]{0:T(128)S(1)} %pad_add_fusion.meta, s32[32]{0:T(128)S(1)} %bitcast.43, s32[32]{0:T(128)S(1)} %bitcast.38, bf16[32,128,128]{2,1,0:T(8,128)(2,1)S(1)} %bitcast.33, bf16[8,64,128]{2,1,0:T(8,128)(2,1)S(1)} %get-tuple-element.60.refs_0_.refs_8_, ...), custom_call_target="tpu_custom_call" | custom-call | flops 67108864 | bytes 2621704 | tf_op jit(solution)/shard_map/pallas_call | solution.py:24
  148.5 1.5 collective-permute-start.65
  154.9 4.9 %custom-call.7 = f32[1,64,64]{1,2,0:T(8,128)S(1)} custom-call(f32[1,64,64]{2,1,0:T(8,128)S(1)} %fusion), custom_call_target="InvertDiagBlocksLowerTriangular" | custom-call | tf_op jit(solution)/shard_map/jit(_solve_triangular)/triangular_solve | solution.py:244
  159.8 2.5 %collective-permute-start.69 = (f32[64,64]{1,0:T(8,128)S(1)}, f32[64,64]{1,0:T(8,128)S(1)}, u32[]{:S(2)}, u32[]{:S(2)}) collective-permute-start(f32[64,64]{1,0:T(8,128)S(1)} %add_add_fusion), channel_id=1, source_target_pairs={{0,24},{8,16},{16,8},{24,0},{1,25},{9,17},{17,9},{25,1},{2,26},{10... | collective-permute-start | bytes 49160 | tf_op jit(solution)/shard_map/ppermute | solution.py:38
  162.3 2.0 %collective-permute-start.67 = (f32[64,64]{1,0:T(8,128)S(1)}, f32[64,64]{1,0:T(8,128)S(1)}, u32[]{:S(2)}, u32[]{:S(2)}) collective-permute-start(f32[64,64]{1,0:T(8,128)S(1)} %add_add_fusion), channel_id=1, source_target_pairs={{0,8},{8,0},{16,24},{24,16},{1,9},{9,1},{17,25},{25,17},{2,10},{10... | collective-permute-start | bytes 49160 | tf_op jit(solution)/shard_map/ppermute | solution.py:38
  (133 shorter events, 39.0 us)
Async XLA Ops:
  5.6 9.0 %collective-permute-start.7 = (bf16[8,64,128]{2,1,0:T(8,128)(2,1)S(1)}, bf16[8,64,128]{2,1,0:T(8,128)(2,1)S(1)}, u32[]{:S(2)}, u32[]{:S(2)}) collective-permute-start(bf16[8,64,128]{2,1,0:T(8,128)(2,1)S(1)} %shard_map.59.refs_0_), channel_id=1, source_target_pairs={{0,5},{1,4},{2,7},{3,6},{4,1},{5,0},{6,3},{7,2},{8,13},{9,12},{10,... | collective-permute-start | bytes 393224 | tf_op jit(solution)/shard_map/ppermute | solution.py:38
  7.0 12.0 %collective-permute-start.6 = (bf16[8,64,128]{2,1,0:T(8,128)(2,1)S(1)}, bf16[8,64,128]{2,1,0:T(8,128)(2,1)S(1)}, u32[]{:S(2)}, u32[]{:S(2)}) collective-permute-start(bf16[8,64,128]{2,1,0:T(8,128)(2,1)S(1)} %shard_map.59.refs_0_), channel_id=1, source_target_pairs={{0,4},{1,5},{2,6},{3,7},{4,0},{5,1},{6,2},{7,3},{8,12},{9,13},{10,... | collective-permute-start | bytes 393224 | tf_op jit(solution)/shard_map/ppermute | solution.py:38
  7.3 13.5 %collective-permute-start.5 = (bf16[8,64,128]{2,1,0:T(8,128)(2,1)S(1)}, bf16[8,64,128]{2,1,0:T(8,128)(2,1)S(1)}, u32[]{:S(2)}, u32[]{:S(2)}) collective-permute-start(bf16[8,64,128]{2,1,0:T(8,128)(2,1)S(1)} %shard_map.59.refs_0_), channel_id=1, source_target_pairs={{0,3},{1,2},{2,1},{3,0},{4,7},{5,6},{6,5},{7,4},{8,11},{9,10},{10,... | collective-permute-start | bytes 393224 | tf_op jit(solution)/shard_map/ppermute | solution.py:38
  8.9 13.7 %collective-permute-start.4 = (bf16[8,64,128]{2,1,0:T(8,128)(2,1)S(1)}, bf16[8,64,128]{2,1,0:T(8,128)(2,1)S(1)}, u32[]{:S(2)}, u32[]{:S(2)}) collective-permute-start(bf16[8,64,128]{2,1,0:T(8,128)(2,1)S(1)} %shard_map.59.refs_0_), channel_id=1, source_target_pairs={{0,2},{1,3},{2,0},{3,1},{4,6},{5,7},{6,4},{7,5},{8,10},{9,11},{10,... | collective-permute-start | bytes 393224 | tf_op jit(solution)/shard_map/ppermute | solution.py:38
  12.3 10.3 %collective-permute-start.3 = (bf16[8,64,128]{2,1,0:T(8,128)(2,1)S(1)}, bf16[8,64,128]{2,1,0:T(8,128)(2,1)S(1)}, u32[]{:S(2)}, u32[]{:S(2)}) collective-permute-start(bf16[8,64,128]{2,1,0:T(8,128)(2,1)S(1)} %shard_map.59.refs_0_), channel_id=1, source_target_pairs={{0,1},{1,0},{2,3},{3,2},{4,5},{5,4},{6,7},{7,6},{8,9},{9,8},{10,11... | collective-permute-start | bytes 393224 | tf_op jit(solution)/shard_map/ppermute | solution.py:38
  14.7 12.8 %collective-permute-start.2 = (bf16[8,64,128]{2,1,0:T(8,128)(2,1)S(1)}, bf16[8,64,128]{2,1,0:T(8,128)(2,1)S(1)}, u32[]{:S(2)}, u32[]{:S(2)}) collective-permute-start(bf16[8,64,128]{2,1,0:T(8,128)(2,1)S(1)} %shard_map.59.refs_0_), channel_id=1, source_target_pairs={{0,24},{8,16},{16,8},{24,0},{1,25},{9,17},{17,9},{25,1},{2,26},{10... | collective-permute-start | bytes 393224 | tf_op jit(solution)/shard_map/ppermute | solution.py:38
  19.0 12.6 %collective-permute-start.1 = (bf16[8,64,128]{2,1,0:T(8,128)(2,1)S(1)}, bf16[8,64,128]{2,1,0:T(8,128)(2,1)S(1)}, u32[]{:S(2)}, u32[]{:S(2)}) collective-permute-start(bf16[8,64,128]{2,1,0:T(8,128)(2,1)S(1)} %shard_map.59.refs_0_), channel_id=1, source_target_pairs={{0,16},{8,24},{16,0},{24,8},{1,17},{9,25},{17,1},{25,9},{2,18},{10... | collective-permute-start | bytes 393224 | tf_op jit(solution)/shard_map/ppermute | solution.py:38
  20.8 10.7 %collective-permute-start = (bf16[8,64,128]{2,1,0:T(8,128)(2,1)S(1)}, bf16[8,64,128]{2,1,0:T(8,128)(2,1)S(1)}, u32[]{:S(2)}, u32[]{:S(2)}) collective-permute-start(bf16[8,64,128]{2,1,0:T(8,128)(2,1)S(1)} %shard_map.59.refs_0_), channel_id=1, source_target_pairs={{0,8},{8,0},{16,24},{24,16},{1,9},{9,1},{17,25},{25,17},{2,10},{10... | collective-permute-start | bytes 393224 | tf_op jit(solution)/shard_map/ppermute | solution.py:38
  25.9 9.5 %collective-permute-start.17 = (bf16[9,64,128]{2,1,0:T(8,128)(2,1)S(1)}, bf16[9,64,128]{2,1,0:T(8,128)(2,1)S(1)}, u32[]{:S(2)}, u32[]{:S(2)}) collective-permute-start(bf16[9,64,128]{2,1,0:T(8,128)(2,1)S(1)} %get-tuple-element.41), channel_id=1, source_target_pairs={{0,8},{8,0},{16,24},{24,16},{1,9},{9,1},{17,25},{25,17},{2,10},{10... | collective-permute-start | bytes 442376 | tf_op jit(solution)/shard_map/ppermute | solution.py:38
  26.4 14.3 %collective-permute-start.18 = (bf16[9,64,128]{2,1,0:T(8,128)(2,1)S(1)}, bf16[9,64,128]{2,1,0:T(8,128)(2,1)S(1)}, u32[]{:S(2)}, u32[]{:S(2)}) collective-permute-start(bf16[9,64,128]{2,1,0:T(8,128)(2,1)S(1)} %get-tuple-element.42), channel_id=1, source_target_pairs={{0,16},{8,24},{16,0},{24,8},{1,17},{9,25},{17,1},{25,9},{2,18},{10... | collective-permute-start | bytes 442376 | tf_op jit(solution)/shard_map/ppermute | solution.py:38
  27.5 14.7 %collective-permute-start.19 = (bf16[9,64,128]{2,1,0:T(8,128)(2,1)S(1)}, bf16[9,64,128]{2,1,0:T(8,128)(2,1)S(1)}, u32[]{:S(2)}, u32[]{:S(2)}) collective-permute-start(bf16[9,64,128]{2,1,0:T(8,128)(2,1)S(1)} %get-tuple-element.43), channel_id=1, source_target_pairs={{0,24},{8,16},{16,8},{24,0},{1,25},{9,17},{17,9},{25,1},{2,26},{10... | collective-permute-start | bytes 442376 | tf_op jit(solution)/shard_map/ppermute | solution.py:38
  33.3 8.9 %collective-permute-start.10 = (bf16[9,64,128]{2,1,0:T(8,128)(2,1)S(1)}, bf16[9,64,128]{2,1,0:T(8,128)(2,1)S(1)}, u32[]{:S(2)}, u32[]{:S(2)}) collective-permute-start(bf16[9,64,128]{2,1,0:T(8,128)(2,1)S(1)} %get-tuple-element.34), channel_id=1, source_target_pairs={{0,1},{1,0},{2,3},{3,2},{4,5},{5,4},{6,7},{7,6},{8,9},{9,8},{10,11... | collective-permute-start | bytes 442376 | tf_op jit(solution)/shard_map/ppermute | solution.py:38
  33.4 10.3 %collective-permute-start.11 = (bf16[9,64,128]{2,1,0:T(8,128)(2,1)S(1)}, bf16[9,64,128]{2,1,0:T(8,128)(2,1)S(1)}, u32[]{:S(2)}, u32[]{:S(2)}) collective-permute-start(bf16[9,64,128]{2,1,0:T(8,128)(2,1)S(1)} %get-tuple-element.35), channel_id=1, source_target_pairs={{0,2},{1,3},{2,0},{3,1},{4,6},{5,7},{6,4},{7,5},{8,10},{9,11},{10,... | collective-permute-start | bytes 442376 | tf_op jit(solution)/shard_map/ppermute | solution.py:38
  35.3 9.8 %collective-permute-start.12 = (bf16[9,64,128]{2,1,0:T(8,128)(2,1)S(1)}, bf16[9,64,128]{2,1,0:T(8,128)(2,1)S(1)}, u32[]{:S(2)}, u32[]{:S(2)}) collective-permute-start(bf16[9,64,128]{2,1,0:T(8,128)(2,1)S(1)} %get-tuple-element.36), channel_id=1, source_target_pairs={{0,3},{1,2},{2,1},{3,0},{4,7},{5,6},{6,5},{7,4},{8,11},{9,10},{10,... | collective-permute-start | bytes 442376 | tf_op jit(solution)/shard_map/ppermute | solution.py:38
  40.7 12.1 %collective-permute-start.13 = (bf16[9,64,128]{2,1,0:T(8,128)(2,1)S(1)}, bf16[9,64,128]{2,1,0:T(8,128)(2,1)S(1)}, u32[]{:S(2)}, u32[]{:S(2)}) collective-permute-start(bf16[9,64,128]{2,1,0:T(8,128)(2,1)S(1)} %get-tuple-element.37), channel_id=1, source_target_pairs={{0,4},{1,5},{2,6},{3,7},{4,0},{5,1},{6,2},{7,3},{8,12},{9,13},{10,... | collective-permute-start | bytes 442376 | tf_op jit(solution)/shard_map/ppermute | solution.py:38
  42.2 12.5 %collective-permute-start.14 = (bf16[9,64,128]{2,1,0:T(8,128)(2,1)S(1)}, bf16[9,64,128]{2,1,0:T(8,128)(2,1)S(1)}, u32[]{:S(2)}, u32[]{:S(2)}) collective-permute-start(bf16[9,64,128]{2,1,0:T(8,128)(2,1)S(1)} %get-tuple-element.38), channel_id=1, source_target_pairs={{0,5},{1,4},{2,7},{3,6},{4,1},{5,0},{6,3},{7,2},{8,13},{9,12},{10,... | collective-permute-start | bytes 442376 | tf_op jit(solution)/shard_map/ppermute | solution.py:38
  42.2 12.4 %collective-permute-start.15 = (bf16[9,64,128]{2,1,0:T(8,128)(2,1)S(1)}, bf16[9,64,128]{2,1,0:T(8,128)(2,1)S(1)}, u32[]{:S(2)}, u32[]{:S(2)}) collective-permute-start(bf16[9,64,128]{2,1,0:T(8,128)(2,1)S(1)} %get-tuple-element.39), channel_id=1, source_target_pairs={{0,6},{1,7},{2,4},{3,5},{4,2},{5,3},{6,0},{7,1},{8,14},{9,15},{10,... | collective-permute-start | bytes 442376 | tf_op jit(solution)/shard_map/ppermute | solution.py:38
  43.7 11.0 %collective-permute-start.16 = (bf16[9,64,128]{2,1,0:T(8,128)(2,1)S(1)}, bf16[9,64,128]{2,1,0:T(8,128)(2,1)S(1)}, u32[]{:S(2)}, u32[]{:S(2)}) collective-permute-start(bf16[9,64,128]{2,1,0:T(8,128)(2,1)S(1)} %get-tuple-element.40), channel_id=1, source_target_pairs={{0,7},{1,6},{2,5},{3,4},{4,3},{5,2},{6,1},{7,0},{8,15},{9,14},{10,... | collective-permute-start | bytes 442376 | tf_op jit(solution)/shard_map/ppermute | solution.py:38
  58.0 9.3 %collective-permute-start.27 = (bf16[8,64,128]{2,1,0:T(8,128)(2,1)S(1)}, bf16[8,64,128]{2,1,0:T(8,128)(2,1)S(1)}, u32[]{:S(2)}, u32[]{:S(2)}) collective-permute-start(bf16[8,64,128]{2,1,0:T(8,128)(2,1)S(1)} %get-tuple-element.46.refs_0_), channel_id=1, source_target_pairs={{0,5},{1,4},{2,7},{3,6},{4,1},{5,0},{6,3},{7,2},{8,13},{9,12},{10,... | collective-permute-start | bytes 393224 | tf_op jit(solution)/shard_map/ppermute | solution.py:38
  58.0 12.1 %collective-permute-start.26 = (bf16[8,64,128]{2,1,0:T(8,128)(2,1)S(1)}, bf16[8,64,128]{2,1,0:T(8,128)(2,1)S(1)}, u32[]{:S(2)}, u32[]{:S(2)}) collective-permute-start(bf16[8,64,128]{2,1,0:T(8,128)(2,1)S(1)} %get-tuple-element.46.refs_0_), channel_id=1, source_target_pairs={{0,4},{1,5},{2,6},{3,7},{4,0},{5,1},{6,2},{7,3},{8,12},{9,13},{10,... | collective-permute-start | bytes 393224 | tf_op jit(solution)/shard_map/ppermute | solution.py:38
  59.5 13.0 %collective-permute-start.25 = (bf16[8,64,128]{2,1,0:T(8,128)(2,1)S(1)}, bf16[8,64,128]{2,1,0:T(8,128)(2,1)S(1)}, u32[]{:S(2)}, u32[]{:S(2)}) collective-permute-start(bf16[8,64,128]{2,1,0:T(8,128)(2,1)S(1)} %get-tuple-element.46.refs_0_), channel_id=1, source_target_pairs={{0,3},{1,2},{2,1},{3,0},{4,7},{5,6},{6,5},{7,4},{8,11},{9,10},{10,... | collective-permute-start | bytes 393224 | tf_op jit(solution)/shard_map/ppermute | solution.py:38
  61.2 11.9 %collective-permute-start.24 = (bf16[8,64,128]{2,1,0:T(8,128)(2,1)S(1)}, bf16[8,64,128]{2,1,0:T(8,128)(2,1)S(1)}, u32[]{:S(2)}, u32[]{:S(2)}) collective-permute-start(bf16[8,64,128]{2,1,0:T(8,128)(2,1)S(1)} %get-tuple-element.46.refs_0_), channel_id=1, source_target_pairs={{0,2},{1,3},{2,0},{3,1},{4,6},{5,7},{6,4},{7,5},{8,10},{9,11},{10,... | collective-permute-start | bytes 393224 | tf_op jit(solution)/shard_map/ppermute | solution.py:38
  65.1 8.0 %collective-permute-start.23 = (bf16[8,64,128]{2,1,0:T(8,128)(2,1)S(1)}, bf16[8,64,128]{2,1,0:T(8,128)(2,1)S(1)}, u32[]{:S(2)}, u32[]{:S(2)}) collective-permute-start(bf16[8,64,128]{2,1,0:T(8,128)(2,1)S(1)} %get-tuple-element.46.refs_0_), channel_id=1, source_target_pairs={{0,1},{1,0},{2,3},{3,2},{4,5},{5,4},{6,7},{7,6},{8,9},{9,8},{10,11... | collective-permute-start | bytes 393224 | tf_op jit(solution)/shard_map/ppermute | solution.py:38
  67.3 9.0 %collective-permute-start.22 = (bf16[8,64,128]{2,1,0:T(8,128)(2,1)S(1)}, bf16[8,64,128]{2,1,0:T(8,128)(2,1)S(1)}, u32[]{:S(2)}, u32[]{:S(2)}) collective-permute-start(bf16[8,64,128]{2,1,0:T(8,128)(2,1)S(1)} %get-tuple-element.46.refs_0_), channel_id=1, source_target_pairs={{0,24},{8,16},{16,8},{24,0},{1,25},{9,17},{17,9},{25,1},{2,26},{10... | collective-permute-start | bytes 393224 | tf_op jit(solution)/shard_map/ppermute | solution.py:38
  70.1 13.4 %collective-permute-start.21 = (bf16[8,64,128]{2,1,0:T(8,128)(2,1)S(1)}, bf16[8,64,128]{2,1,0:T(8,128)(2,1)S(1)}, u32[]{:S(2)}, u32[]{:S(2)}) collective-permute-start(bf16[8,64,128]{2,1,0:T(8,128)(2,1)S(1)} %get-tuple-element.46.refs_0_), channel_id=1, source_target_pairs={{0,16},{8,24},{16,0},{24,8},{1,17},{9,25},{17,1},{25,9},{2,18},{10... | collective-permute-start | bytes 393224 | tf_op jit(solution)/shard_map/ppermute | solution.py:38
  72.5 11.0 %collective-permute-start.20 = (bf16[8,64,128]{2,1,0:T(8,128)(2,1)S(1)}, bf16[8,64,128]{2,1,0:T(8,128)(2,1)S(1)}, u32[]{:S(2)}, u32[]{:S(2)}) collective-permute-start(bf16[8,64,128]{2,1,0:T(8,128)(2,1)S(1)} %get-tuple-element.46.refs_0_), channel_id=1, source_target_pairs={{0,8},{8,0},{16,24},{24,16},{1,9},{9,1},{17,25},{25,17},{2,10},{10... | collective-permute-start | bytes 393224 | tf_op jit(solution)/shard_map/ppermute | solution.py:38
  74.3 12.3 %collective-permute-start.37 = (bf16[8,64,128]{2,1,0:T(8,128)(2,1)S(1)}, bf16[8,64,128]{2,1,0:T(8,128)(2,1)S(1)}, u32[]{:S(2)}, u32[]{:S(2)}) collective-permute-start(bf16[8,64,128]{2,1,0:T(8,128)(2,1)S(1)} %get-tuple-element.56), channel_id=1, source_target_pairs={{0,8},{8,0},{16,24},{24,16},{1,9},{9,1},{17,25},{25,17},{2,10},{10... | collective-permute-start | bytes 393224 | tf_op jit(solution)/shard_map/ppermute | solution.py:38
  75.8 15.5 %collective-permute-start.38 = (bf16[8,64,128]{2,1,0:T(8,128)(2,1)S(1)}, bf16[8,64,128]{2,1,0:T(8,128)(2,1)S(1)}, u32[]{:S(2)}, u32[]{:S(2)}) collective-permute-start(bf16[8,64,128]{2,1,0:T(8,128)(2,1)S(1)} %get-tuple-element.57), channel_id=1, source_target_pairs={{0,16},{8,24},{16,0},{24,8},{1,17},{9,25},{17,1},{25,9},{2,18},{10... | collective-permute-start | bytes 393224 | tf_op jit(solution)/shard_map/ppermute | solution.py:38
  76.3 15.9 %collective-permute-start.39 = (bf16[8,64,128]{2,1,0:T(8,128)(2,1)S(1)}, bf16[8,64,128]{2,1,0:T(8,128)(2,1)S(1)}, u32[]{:S(2)}, u32[]{:S(2)}) collective-permute-start(bf16[8,64,128]{2,1,0:T(8,128)(2,1)S(1)} %get-tuple-element.58), channel_id=1, source_target_pairs={{0,24},{8,16},{16,8},{24,0},{1,25},{9,17},{17,9},{25,1},{2,26},{10... | collective-permute-start | bytes 393224 | tf_op jit(solution)/shard_map/ppermute | solution.py:38
  85.0 9.4 %collective-permute-start.31 = (bf16[8,64,128]{2,1,0:T(8,128)(2,1)S(1)}, bf16[8,64,128]{2,1,0:T(8,128)(2,1)S(1)}, u32[]{:S(2)}, u32[]{:S(2)}) collective-permute-start(bf16[8,64,128]{2,1,0:T(8,128)(2,1)S(1)} %get-tuple-element.50), channel_id=1, source_target_pairs={{0,2},{1,3},{2,0},{3,1},{4,6},{5,7},{6,4},{7,5},{8,10},{9,11},{10,... | collective-permute-start | bytes 393224 | tf_op jit(solution)/shard_map/ppermute | solution.py:38
  86.7 9.1 %collective-permute-start.32 = (bf16[8,64,128]{2,1,0:T(8,128)(2,1)S(1)}, bf16[8,64,128]{2,1,0:T(8,128)(2,1)S(1)}, u32[]{:S(2)}, u32[]{:S(2)}) collective-permute-start(bf16[8,64,128]{2,1,0:T(8,128)(2,1)S(1)} %get-tuple-element.51), channel_id=1, source_target_pairs={{0,3},{1,2},{2,1},{3,0},{4,7},{5,6},{6,5},{7,4},{8,11},{9,10},{10,... | collective-permute-start | bytes 393224 | tf_op jit(solution)/shard_map/ppermute | solution.py:38
  91.3 11.7 %collective-permute-start.33 = (bf16[8,64,128]{2,1,0:T(8,128)(2,1)S(1)}, bf16[8,64,128]{2,1,0:T(8,128)(2,1)S(1)}, u32[]{:S(2)}, u32[]{:S(2)}) collective-permute-start(bf16[8,64,128]{2,1,0:T(8,128)(2,1)S(1)} %get-tuple-element.52), channel_id=1, source_target_pairs={{0,4},{1,5},{2,6},{3,7},{4,0},{5,1},{6,2},{7,3},{8,12},{9,13},{10,... | collective-permute-start | bytes 393224 | tf_op jit(solution)/shard_map/ppermute | solution.py:38
  92.2 11.4 %collective-permute-start.34 = (bf16[8,64,128]{2,1,0:T(8,128)(2,1)S(1)}, bf16[8,64,128]{2,1,0:T(8,128)(2,1)S(1)}, u32[]{:S(2)}, u32[]{:S(2)}) collective-permute-start(bf16[8,64,128]{2,1,0:T(8,128)(2,1)S(1)} %get-tuple-element.53), channel_id=1, source_target_pairs={{0,5},{1,4},{2,7},{3,6},{4,1},{5,0},{6,3},{7,2},{8,13},{9,12},{10,... | collective-permute-start | bytes 393224 | tf_op jit(solution)/shard_map/ppermute | solution.py:38
  92.2 11.4 %collective-permute-start.35 = (bf16[8,64,128]{2,1,0:T(8,128)(2,1)S(1)}, bf16[8,64,128]{2,1,0:T(8,128)(2,1)S(1)}, u32[]{:S(2)}, u32[]{:S(2)}) collective-permute-start(bf16[8,64,128]{2,1,0:T(8,128)(2,1)S(1)} %get-tuple-element.54), channel_id=1, source_target_pairs={{0,6},{1,7},{2,4},{3,5},{4,2},{5,3},{6,0},{7,1},{8,14},{9,15},{10,... | collective-permute-start | bytes 393224 | tf_op jit(solution)/shard_map/ppermute | solution.py:38
  94.4 9.2 %collective-permute-start.36 = (bf16[8,64,128]{2,1,0:T(8,128)(2,1)S(1)}, bf16[8,64,128]{2,1,0:T(8,128)(2,1)S(1)}, u32[]{:S(2)}, u32[]{:S(2)}) collective-permute-start(bf16[8,64,128]{2,1,0:T(8,128)(2,1)S(1)} %get-tuple-element.55), channel_id=1, source_target_pairs={{0,7},{1,6},{2,5},{3,4},{4,3},{5,2},{6,1},{7,0},{8,15},{9,14},{10,... | collective-permute-start | bytes 393224 | tf_op jit(solution)/shard_map/ppermute | solution.py:38
  117.5 8.1 %collective-permute-start.48 = (f32[64,128]{1,0:T(8,128)S(1)}, f32[64,128]{1,0:T(8,128)S(1)}, u32[]{:S(2)}, u32[]{:S(2)}) collective-permute-start(f32[64,128]{1,0:T(8,128)S(1)} %add_add_fusion.1), channel_id=1, source_target_pairs={{0,16},{8,24},{16,0},{24,8},{1,17},{9,25},{17,1},{25,9},{2,18},{10... | collective-permute-start | bytes 98312 | tf_op jit(solution)/shard_map/ppermute | solution.py:38
  117.5 8.1 %collective-permute-start.47 = (f32[64,128]{1,0:T(8,128)S(1)}, f32[64,128]{1,0:T(8,128)S(1)}, u32[]{:S(2)}, u32[]{:S(2)}) collective-permute-start(f32[64,128]{1,0:T(8,128)S(1)} %add_add_fusion.1), channel_id=1, source_target_pairs={{0,8},{8,0},{16,24},{24,16},{1,9},{9,1},{17,25},{25,17},{2,10},{10... | collective-permute-start | bytes 98312 | tf_op jit(solution)/shard_map/ppermute | solution.py:38
  119.4 8.3 %collective-permute-start.59 = (bf16[8,64,128]{2,1,0:T(8,128)(2,1)S(1)}, bf16[8,64,128]{2,1,0:T(8,128)(2,1)S(1)}, u32[]{:S(2)}, u32[]{:S(2)}) collective-permute-start(bf16[8,64,128]{2,1,0:T(8,128)(2,1)S(1)} %get-tuple-element.60.refs_0_.refs_8_), channel_id=1, source_target_pairs={{0,24},{8,16},{16,8},{24,0},{1,25},{9,17},{17,9},{25,1},{2,26},{10... | collective-permute-start | bytes 393224 | tf_op jit(solution)/shard_map/ppermute | solution.py:38
  121.9 10.4 %collective-permute-start.58 = (bf16[8,64,128]{2,1,0:T(8,128)(2,1)S(1)}, bf16[8,64,128]{2,1,0:T(8,128)(2,1)S(1)}, u32[]{:S(2)}, u32[]{:S(2)}) collective-permute-start(bf16[8,64,128]{2,1,0:T(8,128)(2,1)S(1)} %get-tuple-element.60.refs_0_.refs_8_), channel_id=1, source_target_pairs={{0,16},{8,24},{16,0},{24,8},{1,17},{9,25},{17,1},{25,9},{2,18},{10... | collective-permute-start | bytes 393224 | tf_op jit(solution)/shard_map/ppermute | solution.py:38
  121.9 11.5 %collective-permute-start.57 = (bf16[8,64,128]{2,1,0:T(8,128)(2,1)S(1)}, bf16[8,64,128]{2,1,0:T(8,128)(2,1)S(1)}, u32[]{:S(2)}, u32[]{:S(2)}) collective-permute-start(bf16[8,64,128]{2,1,0:T(8,128)(2,1)S(1)} %get-tuple-element.60.refs_0_.refs_8_), channel_id=1, source_target_pairs={{0,8},{8,0},{16,24},{24,16},{1,9},{9,1},{17,25},{25,17},{2,10},{10... | collective-permute-start | bytes 393224 | tf_op jit(solution)/shard_map/ppermute | solution.py:38
  125.6 7.8 %collective-permute-start.56 = (bf16[8,64,128]{2,1,0:T(8,128)(2,1)S(1)}, bf16[8,64,128]{2,1,0:T(8,128)(2,1)S(1)}, u32[]{:S(2)}, u32[]{:S(2)}) collective-permute-start(bf16[8,64,128]{2,1,0:T(8,128)(2,1)S(1)} %get-tuple-element.60.refs_0_.refs_8_), channel_id=1, source_target_pairs={{0,7},{1,6},{2,5},{3,4},{4,3},{5,2},{6,1},{7,0},{8,15},{9,14},{10,... | collective-permute-start | bytes 393224 | tf_op jit(solution)/shard_map/ppermute | solution.py:38
  125.6 9.0 %collective-permute-start.55 = (bf16[8,64,128]{2,1,0:T(8,128)(2,1)S(1)}, bf16[8,64,128]{2,1,0:T(8,128)(2,1)S(1)}, u32[]{:S(2)}, u32[]{:S(2)}) collective-permute-start(bf16[8,64,128]{2,1,0:T(8,128)(2,1)S(1)} %get-tuple-element.60.refs_0_.refs_8_), channel_id=1, source_target_pairs={{0,6},{1,7},{2,4},{3,5},{4,2},{5,3},{6,0},{7,1},{8,14},{9,15},{10,... | collective-permute-start | bytes 393224 | tf_op jit(solution)/shard_map/ppermute | solution.py:38
  127.7 13.5 %collective-permute-start.54 = (bf16[8,64,128]{2,1,0:T(8,128)(2,1)S(1)}, bf16[8,64,128]{2,1,0:T(8,128)(2,1)S(1)}, u32[]{:S(2)}, u32[]{:S(2)}) collective-permute-start(bf16[8,64,128]{2,1,0:T(8,128)(2,1)S(1)} %get-tuple-element.60.refs_0_.refs_8_), channel_id=1, source_target_pairs={{0,5},{1,4},{2,7},{3,6},{4,1},{5,0},{6,3},{7,2},{8,13},{9,12},{10,... | collective-permute-start | bytes 393224 | tf_op jit(solution)/shard_map/ppermute | solution.py:38
  132.3 8.9 %collective-permute-start.53 = (bf16[8,64,128]{2,1,0:T(8,128)(2,1)S(1)}, bf16[8,64,128]{2,1,0:T(8,128)(2,1)S(1)}, u32[]{:S(2)}, u32[]{:S(2)}) collective-permute-start(bf16[8,64,128]{2,1,0:T(8,128)(2,1)S(1)} %get-tuple-element.60.refs_0_.refs_8_), channel_id=1, source_target_pairs={{0,4},{1,5},{2,6},{3,7},{4,0},{5,1},{6,2},{7,3},{8,12},{9,13},{10,... | collective-permute-start | bytes 393224 | tf_op jit(solution)/shard_map/ppermute | solution.py:38
  133.4 7.8 %collective-permute-start.52 = (bf16[8,64,128]{2,1,0:T(8,128)(2,1)S(1)}, bf16[8,64,128]{2,1,0:T(8,128)(2,1)S(1)}, u32[]{:S(2)}, u32[]{:S(2)}) collective-permute-start(bf16[8,64,128]{2,1,0:T(8,128)(2,1)S(1)} %get-tuple-element.60.refs_0_.refs_8_), channel_id=1, source_target_pairs={{0,3},{1,2},{2,1},{3,0},{4,7},{5,6},{6,5},{7,4},{8,11},{9,10},{10,... | collective-permute-start | bytes 393224 | tf_op jit(solution)/shard_map/ppermute | solution.py:38
  133.4 7.8 %collective-permute-start.51 = (bf16[8,64,128]{2,1,0:T(8,128)(2,1)S(1)}, bf16[8,64,128]{2,1,0:T(8,128)(2,1)S(1)}, u32[]{:S(2)}, u32[]{:S(2)}) collective-permute-start(bf16[8,64,128]{2,1,0:T(8,128)(2,1)S(1)} %get-tuple-element.60.refs_0_.refs_8_), channel_id=1, source_target_pairs={{0,2},{1,3},{2,0},{3,1},{4,6},{5,7},{6,4},{7,5},{8,10},{9,11},{10,... | collective-permute-start | bytes 393224 | tf_op jit(solution)/shard_map/ppermute | solution.py:38
  150.6 9.2 %collective-permute-start.64 = (f32[64,64]{1,0:T(8,128)S(1)}, f32[64,64]{1,0:T(8,128)S(1)}, u32[]{:S(2)}, u32[]{:S(2)}) collective-permute-start(f32[64,64]{1,0:T(8,128)S(1)} %shard_map.66), channel_id=1, source_target_pairs={{0,5},{1,4},{2,7},{3,6},{4,1},{5,0},{6,3},{7,2},{8,13},{9,12},{10,... | collective-permute-start | bytes 49160 | tf_op jit(solution)/shard_map/ppermute | solution.py:38
  151.6 8.2 %collective-permute-start.63 = (f32[64,64]{1,0:T(8,128)S(1)}, f32[64,64]{1,0:T(8,128)S(1)}, u32[]{:S(2)}, u32[]{:S(2)}) collective-permute-start(f32[64,64]{1,0:T(8,128)S(1)} %shard_map.66), channel_id=1, source_target_pairs={{0,4},{1,5},{2,6},{3,7},{4,0},{5,1},{6,2},{7,3},{8,12},{9,13},{10,... | collective-permute-start | bytes 49160 | tf_op jit(solution)/shard_map/ppermute | solution.py:38
  (29 other events, 165.2 us)

commit v2 on v1

v2 whole, which is shorter than its diff:
```python
import functools

import jax
import jax.numpy as jnp
from jax import lax
from jax.experimental import pallas as pl
from jax.experimental.pallas import tpu as pltpu
from jax.sharding import PartitionSpec as P

CENTER = 1.0
HALF_WIDTH = 0.5
HIGHEST = lax.Precision.HIGHEST
NT = (((1,), (1,)), ((), ()))
NN = (((1,), (0,)), ((), ()))
BF16 = jnp.bfloat16
F32 = jnp.float32
VMEM = pl.BlockSpec(memory_space=pltpu.VMEM)
SMEM = pl.BlockSpec(memory_space=pltpu.SMEM)
DEGREE_ROWS = 16


def call(kernel, out_shape, scratch, limit, args, flops=0, smem=0):
    moved = sum(x.size * x.dtype.itemsize for x in args)
    return pl.pallas_call(
        kernel,
        out_shape=out_shape,
        in_specs=[SMEM] * smem + [VMEM] * (len(args) - smem),
        out_specs=jax.tree.map(lambda _: VMEM, out_shape),
        scratch_shapes=scratch,
        compiler_params=pltpu.CompilerParams(vmem_limit_bytes=limit * 2**20),
        cost_estimate=pl.CostEstimate(flops=flops, bytes_accessed=moved, transcendentals=0),
    )(*args)


def swap(parts, axis):
    return lax.all_to_all(parts, axis, 0, 0, tiled=True)


def exchange(parts, axis):
    n = lax.axis_size(axis)
    return [
        lax.ppermute(part, axis, [(i, i ^ d) for i in range(n)])
        for d, part in zip(range(1, n), parts)
    ]


def tiles_first(ref, width):
    return [ref[:, k * width : (k + 1) * width] for k in range(ref.shape[1] // width)]


def round_kernel(vec_ref, *out_refs):
    width = out_refs[0].shape[3]
    for k, piece in enumerate(tiles_first(vec_ref, width)):
        store_copies(out_refs, k, piece.astype(BF16))


def store_copies(out_refs, k, piece):
    for out in out_refs:
        for d in range(out.shape[0]):
            out[d, k] = piece


def product_kernel(degree, dims, meta, in_rows, out_rows, tiles_ref, parts_ref, own_ref, send_ref, panel, total):
    parts_n, group, vectors_n, width = parts_ref.shape
    for d in range(parts_n):
        panel[d * group : (d + 1) * group, :vectors_n, :] = parts_ref[d]
    if degree:
        panel[:, vectors_n:, :] = jnp.ones(
            (panel.shape[0], panel.shape[1] - vectors_n, width), BF16
        )
    total[...] = jnp.zeros_like(total)
    for t in range(tiles_ref.shape[0]):
        total[out_rows[t]] += lax.dot_general(
            panel[in_rows[t]], tiles_ref[t], dims, preferred_element_type=F32
        )
    own_ref[...] = total[pl.ds(meta[0] * group, group)]
    for d in range(send_ref.shape[0]):
        send_ref[d, :group] = total[d * group : (d + 1) * group, :vectors_n, :].astype(BF16)
        if degree:
            sums = jnp.concatenate(
                [total[d * group + k, vectors_n : vectors_n + 1, :] for k in range(group)], 0
            )
            high = sums.astype(BF16).astype(F32)
            low = (sums - high).astype(BF16).astype(F32)
            rest = sums - high - low
            pad = jnp.zeros((vectors_n - 3 * group, width), F32)
            send_ref[d, group] = jnp.concatenate([high, low, rest, pad], 0).astype(BF16)
    send_ref[meta[0]] = jnp.zeros(send_ref.shape[1:], BF16)


def products(tiles, in_rows, out_rows, meta, parts, out_n, dims, degree):
    parts_n, group, vectors_n, width = parts.shape
    height = vectors_n + (DEGREE_ROWS if degree else 0)
    blocks = group + (1 if degree else 0)
    out_shape = [
        jax.ShapeDtypeStruct((group, height, width), F32),
        jax.ShapeDtypeStruct((out_n, blocks, vectors_n, width), BF16),
    ]
    scratch = [
        pltpu.VMEM((parts_n * group, height, width), BF16),
        pltpu.VMEM((out_n * group, height, width), F32),
    ]
    kernel = functools.partial(product_kernel, degree, dims)
    flops = 2 * tiles.size * height
    args = [meta, in_rows, out_rows, tiles, parts]
    return call(kernel, out_shape, scratch, 24, args, flops, 3)


def gathered_sum(own, received, k, rows):
    total = own[k, rows, :]
    for d in range(received.shape[0]):
        total = total + received[d, k, rows, :].astype(F32)
    return total


def first_kernel(vec_ref, row_own, row_got, col_own, col_got, first_ref, degree_ref, *out_refs):
    group, vectors_n, width = out_refs[0].shape[1:]
    degree = jnp.zeros((group, width), F32)
    for own, received in ((row_own, row_got), (col_own, col_got)):
        degree += jnp.concatenate(
            [own[k, vectors_n : vectors_n + 1, :] for k in range(group)], 0
        )
        for d in range(received.shape[0]):
            block = received[d, group].astype(F32)
            degree += (block[2 * group : 3 * group] + block[group : 2 * group]) + block[:group]
    degree = 0.5 * degree
    degree_ref[...] = degree
    every = slice(0, vectors_n)
    for k, vec in enumerate(tiles_first(vec_ref, width)):
        symmetric = 0.5 * (
            gathered_sum(row_own, row_got, k, every) + gathered_sum(col_own, col_got, k, every)
        )
        image = degree[k : k + 1, :] * vec - symmetric
        first = (image - CENTER * vec) / HALF_WIDTH
        first_ref[:, k * width : (k + 1) * width] = first
        store_copies(out_refs, k, first.astype(BF16))


def filter_kernel(
    start_ref, first_ref, degree_ref, row_own, row_got, col_own, col_got, filtered_ref, gram_ref, *refs
):
    out_refs, both = refs[:-1], refs[-1]
    group, vectors_n, width = out_refs[0].shape[1:]
    every = slice(0, vectors_n)
    for k, vec in enumerate(tiles_first(first_ref, width)):
        symmetric = 0.5 * (
            gathered_sum(row_own, row_got, k, every) + gathered_sum(col_own, col_got, k, every)
        )
        columns = slice(k * width, (k + 1) * width)
        image = degree_ref[k : k + 1, :] * vec - symmetric
        filtered = 2.0 * (image - CENTER * vec) / HALF_WIDTH - start_ref[:, columns]
        filtered_ref[:, columns] = filtered
        store_copies(out_refs, k, filtered.astype(BF16))
        both[:vectors_n, columns] = filtered
        both[vectors_n:, columns] = degree_ref[k : k + 1, :] * filtered
    gram_ref[...] = lax.dot_general(
        filtered_ref[...], both[...], NT, precision=HIGHEST, preferred_element_type=F32
    )


def form_kernel(tile_rows, tile_cols, tiles_ref, row_parts, col_parts, out_ref, total):
    group = row_parts.shape[1]
    total[...] = jnp.zeros_like(total)
    for t in range(tiles_ref.shape[0]):
        row, col = tile_rows[t], tile_cols[t]
        product = lax.dot_general(
            col_parts[col // group, col % group], tiles_ref[t], NT, preferred_element_type=F32
        )
        total[...] += lax.dot_general(
            row_parts[row // group, row % group],
            product.astype(BF16),
            NT,
            preferred_element_type=F32,
        )
    out_ref[...] = total[...]


def tree_sum(parts):
    while len(parts) > 1:
        parts = [a + b for a, b in zip(parts[::2], parts[1::2])]
    return parts[0]


def all_sum(part):
    for axis in ("col", "row"):
        n = lax.axis_size(axis)
        part = tree_sum([part, *exchange([part] * (n - 1), axis)])
    return part


def local(tiles, tile_rows, tile_cols, start):
    tiles, tile_rows, tile_cols = tiles[0, 0], tile_rows[0, 0], tile_cols[0, 0]
    width = tiles.shape[-1]
    vectors_n, own_nodes = start.shape
    rows_n, cols_n = lax.axis_size("row"), lax.axis_size("col")
    total_nodes = own_nodes * rows_n * cols_n
    group = own_nodes // width
    row_me = lax.axis_index("row").astype(jnp.int32)[None]
    col_me = lax.axis_index("col").astype(jnp.int32)[None]

    rounded_shapes = [
        jax.ShapeDtypeStruct((n, group, vectors_n, width), BF16) for n in (rows_n, cols_n)
    ]
    vector_shape = jax.ShapeDtypeStruct((vectors_n, own_nodes), F32)

    def apply(to_rows, to_cols, degree):
        col_parts = swap(to_rows, "row")
        row_parts = swap(to_cols, "col")
        row_own, row_send = products(
            tiles, tile_cols, tile_rows, col_me, col_parts, cols_n, NT, degree
        )
        col_own, col_send = products(
            tiles, tile_rows, tile_cols, row_me, row_parts, rows_n, NN, degree
        )
        return [row_own, swap(row_send, "col"), col_own, swap(col_send, "row")]

    rounded = call(round_kernel, rounded_shapes, [], 16, [start])
    sums = apply(*rounded, True)
    first, degree, *rounded = call(
        first_kernel,
        [vector_shape, jax.ShapeDtypeStruct((group, width), F32), *rounded_shapes],
        [],
        24,
        [start, *sums],
    )
    sums = apply(*rounded, False)
    filtered, gram, *rounded = call(
        filter_kernel,
        [
            vector_shape,
            jax.ShapeDtypeStruct((vectors_n, 2 * vectors_n), F32),
            *rounded_shapes,
        ],
        [pltpu.VMEM((2 * vectors_n, own_nodes), F32)],
        24,
        [start, first, degree, *sums],
    )
    col_parts, row_parts = swap(rounded[0], "row"), swap(rounded[1], "col")
    gram = all_sum(gram) / total_nodes
    factor = jnp.linalg.cholesky(gram[:, :vectors_n])
    inverse = jax.scipy.linalg.solve_triangular(
        factor, jnp.eye(vectors_n, dtype=F32), lower=True
    )
    form = call(
        form_kernel,
        jax.ShapeDtypeStruct((vectors_n, vectors_n), F32),
        [pltpu.VMEM((vectors_n, vectors_n), F32)],
        24,
        [tile_rows, tile_cols, tiles, row_parts, col_parts],
        2 * tiles.size * vectors_n,
        2,
    )
    form = all_sum(form) / total_nodes
    projected = gram[:, vectors_n:] - 0.5 * (form + form.T)
    rayleigh = jnp.dot(
        jnp.dot(inverse, projected, precision=HIGHEST), inverse.T, precision=HIGHEST
    )
    ritz = jnp.dot(
        jnp.dot(rayleigh.T, inverse, precision=HIGHEST), filtered, precision=HIGHEST
    )
    return (ritz, rayleigh)


def solution(mesh):
    placed = (
        P("row", "col", None, None, None),
        P("row", "col", None),
        P("row", "col", None),
        P(None, ("row", "col")),
    )
    return jax.shard_map(
        local, mesh=mesh, in_specs=placed, out_specs=(P(None, ("row", "col")), P()), check_vma=False
    )
```

time: 170 us -> 234 us (1.38)
  blocking collectives: 0 us -> 93 us
  starting transfers between devices: 85.8 us -> 40.6 us
  waiting for transfers between devices: 52.2 us -> 65.4 us
    all_to_all x0 -> x5, blocking collectives: none -> 93 us  [swap(): return lax.all_to_all(parts, axis, 0, 0, tiled=True)]
    ppermute x70 -> x20, starting transfers between devices: 85.8 us -> 21.8 us  [exchange(): lax.ppermute(part, axis, [(i, i ^ d) for i in range(n)])]
    all_to_all x0 -> x5, waiting for transfers between devices: none -> 47.4 us  [swap(): return lax.all_to_all(parts, axis, 0, 0, tiled=True)]
    ppermute x70 -> x20, waiting for transfers between devices: 52.2 us -> 18 us  [exchange(): lax.ppermute(part, axis, [(i, i ^ d) for i in range(n)])]
    all_to_all x0 -> x5, starting transfers between devices: none -> 18.8 us  [swap(): return lax.all_to_all(parts, axis, 0, 0, tiled=True)]
  transfers between devices with their start and end apart: 70 -> 25, of which waited for: 25 -> 12; matrix products, arithmetic and copies ran while one was open for 7% -> 5% of each run, Pallas kernels for 3% -> 3%
where the time goes in v2:
time: 234 us; the launch traced here: 233 us
  blocking collectives  93 us (40%)
  waiting for transfers between devices  65.4 us (28%)
  starting transfers between devices  40.6 us (17%)
  Pallas kernels  14.6 us (6%)
  other arithmetic  12.1 us (5%)
  local copies, waits for them, and re-layouts  4.41 us (2%)
    all_to_all x5, blocking collectives, swap(): return lax.all_to_all(parts, axis, 0, 0, tiled=True)  93 us
    all_to_all x5, waiting for transfers between devices, swap(): return lax.all_to_all(parts, axis, 0, 0, tiled=True)  47.4 us
    ppermute x20, starting transfers between devices, exchange(): lax.ppermute(part, axis, [(i, i ^ d) for i in range(n)])  21.8 us
    all_to_all x5, starting transfers between devices, swap(): return lax.all_to_all(parts, axis, 0, 0, tiled=True)  18.8 us
    ppermute x20, waiting for transfers between devices, exchange(): lax.ppermute(part, axis, [(i, i ^ d) for i in range(n)])  18 us
    pallas_call x8, Pallas kernels, call(): pl.pallas_call(kernel, out_shape=out_shape, in_specs=[SMEM] * smem + [VME...  14.6 us
    another operation x3, other arithmetic, local(): factor = jnp.linalg.cholesky(gram[:, :vectors_n])  6.51 us
    another operation x2, other arithmetic, local(): jax.scipy.linalg.solve_triangular(factor, jnp.eye(vectors_n, dtype=F32),...  5.55 us
  transfers between devices with their start and end apart: 25, of which 12 were waited for; matrix products, arithmetic and copies ran while one was open for 5% of the time, Pallas kernels for 3%

profile of v2, /device:TPU:0, one launch (start us, length us, event | category | flops | bytes accessed | tf_op | source)
XLA Modules:
  0.0 233.1 jit_solution(9518042364274279397)
XLA Ops:
  0.6 0.9 copy-done.1
  1.6 0.9 shard_map.59
  2.5 20.4 %all_to_all.50.parts_ref = bf16[8,8,64,128]{3,2,1,0:T(8,128)(2,1)S(1)} all-to-all(bf16[8,8,64,128]{3,2,1,0:T(8,128)(2,1)S(1)} %get-tuple-element.23), channel_id=1, replica_groups=mesh['row'=4,'col'=8] {'col'}, dimensions={0} | all-to-all | bytes 2097152 | tf_op jit(solution)/shard_map/all_to_all | solution.py:36
  23.0 4.9 %all-to-all-start = ((bf16[4,8,64,128]{3,2,1,0:T(8,128)(2,1)}), bf16[4,8,64,128]{3,2,1,0:T(8,128)(2,1)S(1)}, u32[]{:S(2)}, u32[]{:S(2)}) async-start(bf16[4,8,64,128]{3,2,1,0:T(8,128)(2,1)} %get-tuple-element.20), calls=%async_computation | async-start | bytes 1048576 | tf_op jit(solution)/shard_map/all_to_all | solution.py:36
  27.9 2.1 shard_map.61
  30.0 11.7 %all-to-all-done.parts_ref = bf16[4,8,64,128]{3,2,1,0:T(8,128)(2,1)S(1)} async-done(((bf16[4,8,64,128]{3,2,1,0:T(8,128)(2,1)}), bf16[4,8,64,128]{3,2,1,0:T(8,128)(2,1)S(1)}, u32[]{:S(2)}, u32[]{:S(2)}) %all-to-all-start) | async-done | bytes 524320 | tf_op jit(solution)/shard_map/all_to_all | solution.py:36
  41.7 3.5 %all-to-all-start.3 = ((bf16[4,9,64,128]{3,2,1,0:T(8,128)(2,1)}), bf16[4,9,64,128]{3,2,1,0:T(8,128)(2,1)S(1)}, u32[]{:S(2)}, u32[]{:S(2)}) async-start(bf16[4,9,64,128]{3,2,1,0:T(8,128)(2,1)} %get-tuple-element.25), calls=%async_computation.3 | async-start | bytes 1179648 | tf_op jit(solution)/shard_map/all_to_all | solution.py:36
  45.2 1.7 shard_map.60
  46.9 1.0 copy-done.3
  48.0 12.6 %all-to-all-done.3.col_got = bf16[4,9,64,128]{3,2,1,0:T(8,128)(2,1)S(1)} async-done(((bf16[4,9,64,128]{3,2,1,0:T(8,128)(2,1)}), bf16[4,9,64,128]{3,2,1,0:T(8,128)(2,1)S(1)}, u32[]{:S(2)}, u32[]{:S(2)}) %all-to-all-start.3) | async-done | bytes 589856 | tf_op jit(solution)/shard_map/all_to_all | solution.py:36
  60.5 20.4 %all_to_all.51.row_got = bf16[8,9,64,128]{3,2,1,0:T(8,128)(2,1)S(1)} all-to-all(bf16[8,9,64,128]{3,2,1,0:T(8,128)(2,1)} %copy-done.3), channel_id=1, replica_groups=mesh['row'=4,'col'=8] {'col'}, dimensions={0} | all-to-all | bytes 2359296 | tf_op jit(solution)/shard_map/all_to_all | solution.py:36
  81.2 17.8 %all_to_all.52.parts_ref = bf16[8,8,64,128]{3,2,1,0:T(8,128)(2,1)S(1)} all-to-all(bf16[8,8,64,128]{3,2,1,0:T(8,128)(2,1)S(1)} %get-tuple-element.31), channel_id=1, replica_groups=mesh['row'=4,'col'=8] {'col'}, dimensions={0} | all-to-all | bytes 2097152 | tf_op jit(solution)/shard_map/all_to_all | solution.py:36
  99.0 3.5 %all-to-all-start.4 = ((bf16[4,8,64,128]{3,2,1,0:T(8,128)(2,1)}), bf16[4,8,64,128]{3,2,1,0:T(8,128)(2,1)S(1)}, u32[]{:S(2)}, u32[]{:S(2)}) async-start(bf16[4,8,64,128]{3,2,1,0:T(8,128)(2,1)} %copy-done.5), calls=%async_computation.4 | async-start | bytes 1048576 | tf_op jit(solution)/shard_map/all_to_all | solution.py:36
  102.5 1.1 shard_map.64
  103.6 0.8 copy-done.6
  104.5 0.7 copy-done.9
  105.2 11.4 %all-to-all-done.4.parts_ref = bf16[4,8,64,128]{3,2,1,0:T(8,128)(2,1)S(1)} async-done(((bf16[4,8,64,128]{3,2,1,0:T(8,128)(2,1)}), bf16[4,8,64,128]{3,2,1,0:T(8,128)(2,1)S(1)}, u32[]{:S(2)}, u32[]{:S(2)}) %all-to-all-start.4) | async-done | bytes 524320 | tf_op jit(solution)/shard_map/all_to_all | solution.py:36
  116.6 3.5 %all-to-all-start.7 = ((bf16[4,8,64,128]{3,2,1,0:T(8,128)(2,1)}), bf16[4,8,64,128]{3,2,1,0:T(8,128)(2,1)S(1)}, u32[]{:S(2)}, u32[]{:S(2)}) async-start(bf16[4,8,64,128]{3,2,1,0:T(8,128)(2,1)} %copy-done.6), calls=%async_computation.7 | async-start | bytes 1048576 | tf_op jit(solution)/shard_map/all_to_all | solution.py:36
  120.1 1.5 shard_map.63
  121.6 0.7 copy-done.11
  122.3 11.7 %all-to-all-done.7.col_got = bf16[4,8,64,128]{3,2,1,0:T(8,128)(2,1)S(1)} async-done(((bf16[4,8,64,128]{3,2,1,0:T(8,128)(2,1)}), bf16[4,8,64,128]{3,2,1,0:T(8,128)(2,1)S(1)}, u32[]{:S(2)}, u32[]{:S(2)}) %all-to-all-start.7) | async-done | bytes 524320 | tf_op jit(solution)/shard_map/all_to_all | solution.py:36
  134.0 17.9 %all_to_all.53.row_got = bf16[8,8,64,128]{3,2,1,0:T(8,128)(2,1)S(1)} all-to-all(bf16[8,8,64,128]{3,2,1,0:T(8,128)(2,1)S(1)} %get-tuple-element.30), channel_id=1, replica_groups=mesh['row'=4,'col'=8] {'col'}, dimensions={0} | all-to-all | bytes 2097152 | tf_op jit(solution)/shard_map/all_to_all | solution.py:36
  151.9 0.9 shard_map.65
  152.9 16.5 %all_to_all.54.col_parts = bf16[4,8,64,128]{3,2,1,0:T(8,128)(2,1)S(1)} all-to-all(bf16[4,8,64,128]{3,2,1,0:T(8,128)(2,1)S(1)} %get-tuple-element.36), channel_id=1, replica_groups=mesh['row'=4,'col'=8] {'row'}, dimensions={0} | all-to-all | bytes 1048576 | tf_op jit(solution)/shard_map/all_to_all | solution.py:36
  169.4 3.6 %all-to-all-start.8 = ((bf16[8,8,64,128]{3,2,1,0:T(8,128)(2,1)}), bf16[8,8,64,128]{3,2,1,0:T(8,128)(2,1)S(1)}, u32[]{:S(2)}, u32[]{:S(2)}) async-start(bf16[8,8,64,128]{3,2,1,0:T(8,128)(2,1)} %copy-done.4), calls=%async_computation.8 | async-start | bytes 2097152 | tf_op jit(solution)/shard_map/all_to_all | solution.py:36
  172.9 2.6 %collective-permute-start.6 = (f32[64,128]{1,0:T(8,128)S(1)}, f32[64,128]{1,0:T(8,128)S(1)}, u32[]{:S(2)}, u32[]{:S(2)}) collective-permute-start(f32[64,128]{1,0:T(8,128)S(1)} %get-tuple-element.34), channel_id=1, source_target_pairs={{0,7},{1,6},{2,5},{3,4},{4,3},{5,2},{6,1},{7,0},{8,15},{9,14},{10,... | collective-permute-start | bytes 98312 | tf_op jit(solution)/shard_map/ppermute | solution.py:42
  175.9 1.4 collective-permute-start.4
  177.6 1.4 collective-permute-start.2
  179.0 9.6 %collective-permute-done.6 = f32[64,128]{1,0:T(8,128)S(1)} collective-permute-done((f32[64,128]{1,0:T(8,128)S(1)}, f32[64,128]{1,0:T(8,128)S(1)}, u32[]{:S(2)}, u32[]{:S(2)}) %collective-permute-start.6) | collective-permute-done | bytes 32800 | tf_op jit(solution)/shard_map/ppermute | solution.py:42
  189.1 1.0 collective-permute-done.5
  190.1 2.5 %collective-permute-done.1 = f32[64,128]{1,0:T(8,128)S(1)} collective-permute-done((f32[64,128]{1,0:T(8,128)S(1)}, f32[64,128]{1,0:T(8,128)S(1)}, u32[]{:S(2)}, u32[]{:S(2)}) %collective-permute-start.1) | collective-permute-done | bytes 32800 | tf_op jit(solution)/shard_map/ppermute | solution.py:42
  192.6 1.5 collective-permute-start.9
  194.4 2.7 %collective-permute-start.7 = (f32[64,128]{1,0:T(8,128)S(1)}, f32[64,128]{1,0:T(8,128)S(1)}, u32[]{:S(2)}, u32[]{:S(2)}) collective-permute-start(f32[64,128]{1,0:T(8,128)S(1)} %add_add_fusion.1), channel_id=1, source_target_pairs={{0,8},{8,0},{16,24},{24,16},{1,9},{9,1},{17,25},{25,17},{2,10},{10... | collective-permute-start | bytes 98312 | tf_op jit(solution)/shard_map/ppermute | solution.py:42
  197.1 1.3 collective-permute-done.9
  198.4 0.9 collective-permute-done.8
  199.4 5.8 %cholesky.17 = f32[64,64]{1,0:T(8,128)S(1)} custom-call(f32[64,64]{1,0:T(8,128)S(1)} %fusion.6), custom_call_target="Cholesky" | custom-call | tf_op jit(solution)/shard_map/jit(cholesky)/cholesky | solution.py:240
  205.3 6.0 %shard_map.66 = f32[64,64]{1,0:T(8,128)S(1)} custom-call(s32[32]{0:T(128)S(1)} %bitcast.43, s32[32]{0:T(128)S(1)} %bitcast.38, bf16[32,128,128]{2,1,0:T(8,128)(2,1)S(1)} %bitcast.33, bf16[8,8,64,128]{3,2,1,0:T(8,128)(2,1)S(1)} %all-to-all-done.8.row_parts, bf16[4,8,64,128]{3,2,1,0:T(8,128)(2,1)S(1)} %all_to_all.54.col_parts), custom_call_target="tpu_custom_call" | custom-call | flops 67108864 | bytes 2621696 | tf_op jit(solution)/shard_map/pallas_call | solution.py:24
  211.4 1.3 collective-permute-start.15
  213.4 1.6 collective-permute-start.14
  214.9 1.5 collective-permute-start.13
  217.0 1.3 collective-permute-start.10
  219.0 4.9 %custom-call.7 = f32[1,64,64]{1,2,0:T(8,128)S(1)} custom-call(f32[1,64,64]{2,1,0:T(8,128)S(1)} %fusion), custom_call_target="InvertDiagBlocksLowerTriangular" | custom-call | tf_op jit(solution)/shard_map/jit(_solve_triangular)/triangular_solve | solution.py:241
  223.9 2.1 collective-permute-start.19
  226.0 1.1 collective-permute-start.18
  227.1 1.3 collective-permute-start.17
  228.6 1.2 collective-permute-done.19
  229.8 1.1 collective-permute-done.18
  232.0 1.1 fusion.11
  (64 shorter events, 5.3 us)
Async XLA Ops:
  0.6 1.0 copy-start.1
  2.5 25.3 %copy-start = (bf16[1,1,32,128,128]{4,3,2,1,0:T(8,128)(2,1)S(1)}, bf16[1,1,32,128,128]{4,3,2,1,0:T(8,128)(2,1)}, u32[]{:S(2)}) copy-start(bf16[1,1,32,128,128]{4,3,2,1,0:T(8,128)(2,1)} %param.4) | copy-start | bytes 3145732
  2.5 25.3 %copy-start.13 = (s32[1,1,32]{2,1,0:T(1,128)S(1)}, s32[1,1,32]{2,1,0:T(1,128)}, u32[]{:S(2)}) copy-start(s32[1,1,32]{2,1,0:T(1,128)} %param.6) | copy-start | bytes 388
  2.5 25.3 %copy-start.14 = (s32[1,1,32]{2,1,0:T(1,128)S(1)}, s32[1,1,32]{2,1,0:T(1,128)}, u32[]{:S(2)}) copy-start(s32[1,1,32]{2,1,0:T(1,128)} %param.5) | copy-start | bytes 388
  23.0 18.7 %all-to-all-start = ((bf16[4,8,64,128]{3,2,1,0:T(8,128)(2,1)}), bf16[4,8,64,128]{3,2,1,0:T(8,128)(2,1)S(1)}, u32[]{:S(2)}, u32[]{:S(2)}) async-start(bf16[4,8,64,128]{3,2,1,0:T(8,128)(2,1)} %get-tuple-element.20), calls=%async_computation | async-start | bytes 1048576 | tf_op jit(solution)/shard_map/all_to_all | solution.py:36
  41.7 18.8 %all-to-all-start.3 = ((bf16[4,9,64,128]{3,2,1,0:T(8,128)(2,1)}), bf16[4,9,64,128]{3,2,1,0:T(8,128)(2,1)S(1)}, u32[]{:S(2)}, u32[]{:S(2)}) async-start(bf16[4,9,64,128]{3,2,1,0:T(8,128)(2,1)} %get-tuple-element.25), calls=%async_computation.3 | async-start | bytes 1179648 | tf_op jit(solution)/shard_map/all_to_all | solution.py:36
  46.9 1.0 copy-start.3
  60.5 20.4 %copy-start.2 = (f32[64,1024]{1,0:T(8,128)S(1)}, f32[64,1024]{1,0:T(8,128)}, u32[]{:S(2)}) copy-start(f32[64,1024]{1,0:T(8,128)} %start_ref.1) | copy-start | bytes 786436
  81.2 17.8 %copy-start.5 = (bf16[4,8,64,128]{3,2,1,0:T(8,128)(2,1)}, bf16[4,8,64,128]{3,2,1,0:T(8,128)(2,1)S(1)}, u32[]{:S(2)}) copy-start(bf16[4,8,64,128]{3,2,1,0:T(8,128)(2,1)S(1)} %get-tuple-element.28) | copy-start | bytes 1572868
  81.2 17.8 %copy-start.7 = (f32[64,1024]{1,0:T(8,128)}, f32[64,1024]{1,0:T(8,128)S(1)}, u32[]{:S(2)}) copy-start(f32[64,1024]{1,0:T(8,128)S(1)} %get-tuple-element.26.first_ref) | copy-start | bytes 786436
  99.0 17.6 %all-to-all-start.4 = ((bf16[4,8,64,128]{3,2,1,0:T(8,128)(2,1)}), bf16[4,8,64,128]{3,2,1,0:T(8,128)(2,1)S(1)}, u32[]{:S(2)}, u32[]{:S(2)}) async-start(bf16[4,8,64,128]{3,2,1,0:T(8,128)(2,1)} %copy-done.5), calls=%async_computation.4 | async-start | bytes 1048576 | tf_op jit(solution)/shard_map/all_to_all | solution.py:36
  103.6 0.8 copy-start.6
  104.5 0.7 copy-start.9
  116.6 17.4 %all-to-all-start.7 = ((bf16[4,8,64,128]{3,2,1,0:T(8,128)(2,1)}), bf16[4,8,64,128]{3,2,1,0:T(8,128)(2,1)S(1)}, u32[]{:S(2)}, u32[]{:S(2)}) async-start(bf16[4,8,64,128]{3,2,1,0:T(8,128)(2,1)} %copy-done.6), calls=%async_computation.7 | async-start | bytes 1048576 | tf_op jit(solution)/shard_map/all_to_all | solution.py:36
  121.6 0.7 copy-start.11
  122.3 29.6 %copy-start.8 = (f32[64,1024]{1,0:T(8,128)S(1)}, f32[64,1024]{1,0:T(8,128)}, u32[]{:S(2)}) copy-start(f32[64,1024]{1,0:T(8,128)} %copy-done.7) | copy-start | bytes 786436
  122.3 29.6 %copy-start.10 = (f32[8,64,128]{2,1,0:T(8,128)S(1)}, f32[8,64,128]{2,1,0:T(8,128)}, u32[]{:S(2)}) copy-start(f32[8,64,128]{2,1,0:T(8,128)} %copy-done.9) | copy-start | bytes 786436
  134.0 17.9 %copy-start.12 = (f32[8,64,128]{2,1,0:T(8,128)S(1)}, f32[8,64,128]{2,1,0:T(8,128)}, u32[]{:S(2)}) copy-start(f32[8,64,128]{2,1,0:T(8,128)} %copy-done.11) | copy-start | bytes 786436
  152.9 16.5 %copy-start.4 = (bf16[8,8,64,128]{3,2,1,0:T(8,128)(2,1)}, bf16[8,8,64,128]{3,2,1,0:T(8,128)(2,1)S(1)}, u32[]{:S(2)}) copy-start(bf16[8,8,64,128]{3,2,1,0:T(8,128)(2,1)S(1)} %get-tuple-element.35) | copy-start | bytes 3145732
  169.4 36.0 %all-to-all-start.8 = ((bf16[8,8,64,128]{3,2,1,0:T(8,128)(2,1)}), bf16[8,8,64,128]{3,2,1,0:T(8,128)(2,1)S(1)}, u32[]{:S(2)}, u32[]{:S(2)}) async-start(bf16[8,8,64,128]{3,2,1,0:T(8,128)(2,1)} %copy-done.4), calls=%async_computation.8 | async-start | bytes 2097152 | tf_op jit(solution)/shard_map/all_to_all | solution.py:36
  172.9 15.7 %collective-permute-start.6 = (f32[64,128]{1,0:T(8,128)S(1)}, f32[64,128]{1,0:T(8,128)S(1)}, u32[]{:S(2)}, u32[]{:S(2)}) collective-permute-start(f32[64,128]{1,0:T(8,128)S(1)} %get-tuple-element.34), channel_id=1, source_target_pairs={{0,7},{1,6},{2,5},{3,4},{4,3},{5,2},{6,1},{7,0},{8,15},{9,14},{10,... | collective-permute-start | bytes 98312 | tf_op jit(solution)/shard_map/ppermute | solution.py:42
  175.6 14.5 %collective-permute-start.5 = (f32[64,128]{1,0:T(8,128)S(1)}, f32[64,128]{1,0:T(8,128)S(1)}, u32[]{:S(2)}, u32[]{:S(2)}) collective-permute-start(f32[64,128]{1,0:T(8,128)S(1)} %get-tuple-element.34), channel_id=1, source_target_pairs={{0,6},{1,7},{2,4},{3,5},{4,2},{5,3},{6,0},{7,1},{8,14},{9,15},{10,... | collective-permute-start | bytes 98312 | tf_op jit(solution)/shard_map/ppermute | solution.py:42
  175.9 14.2 %collective-permute-start.4 = (f32[64,128]{1,0:T(8,128)S(1)}, f32[64,128]{1,0:T(8,128)S(1)}, u32[]{:S(2)}, u32[]{:S(2)}) collective-permute-start(f32[64,128]{1,0:T(8,128)S(1)} %get-tuple-element.34), channel_id=1, source_target_pairs={{0,5},{1,4},{2,7},{3,6},{4,1},{5,0},{6,3},{7,2},{8,13},{9,12},{10,... | collective-permute-start | bytes 98312 | tf_op jit(solution)/shard_map/ppermute | solution.py:42
  177.3 12.9 %collective-permute-start.3 = (f32[64,128]{1,0:T(8,128)S(1)}, f32[64,128]{1,0:T(8,128)S(1)}, u32[]{:S(2)}, u32[]{:S(2)}) collective-permute-start(f32[64,128]{1,0:T(8,128)S(1)} %get-tuple-element.34), channel_id=1, source_target_pairs={{0,4},{1,5},{2,6},{3,7},{4,0},{5,1},{6,2},{7,3},{8,12},{9,13},{10,... | collective-permute-start | bytes 98312 | tf_op jit(solution)/shard_map/ppermute | solution.py:42
  177.6 12.5 %collective-permute-start.2 = (f32[64,128]{1,0:T(8,128)S(1)}, f32[64,128]{1,0:T(8,128)S(1)}, u32[]{:S(2)}, u32[]{:S(2)}) collective-permute-start(f32[64,128]{1,0:T(8,128)S(1)} %get-tuple-element.34), channel_id=1, source_target_pairs={{0,3},{1,2},{2,1},{3,0},{4,7},{5,6},{6,5},{7,4},{8,11},{9,10},{10,... | collective-permute-start | bytes 98312 | tf_op jit(solution)/shard_map/ppermute | solution.py:42
  188.6 4.0 %collective-permute-start.1 = (f32[64,128]{1,0:T(8,128)S(1)}, f32[64,128]{1,0:T(8,128)S(1)}, u32[]{:S(2)}, u32[]{:S(2)}) collective-permute-start(f32[64,128]{1,0:T(8,128)S(1)} %get-tuple-element.34), channel_id=1, source_target_pairs={{0,2},{1,3},{2,0},{3,1},{4,6},{5,7},{6,4},{7,5},{8,10},{9,11},{10,... | collective-permute-start | bytes 98312 | tf_op jit(solution)/shard_map/ppermute | solution.py:42
  190.1 2.5 %collective-permute-start = (f32[64,128]{1,0:T(8,128)S(1)}, f32[64,128]{1,0:T(8,128)S(1)}, u32[]{:S(2)}, u32[]{:S(2)}) collective-permute-start(f32[64,128]{1,0:T(8,128)S(1)} %get-tuple-element.34), channel_id=1, source_target_pairs={{0,1},{1,0},{2,3},{3,2},{4,5},{5,4},{6,7},{7,6},{8,9},{9,8},{10,11... | collective-permute-start | bytes 98312 | tf_op jit(solution)/shard_map/ppermute | solution.py:42
  192.6 5.8 %collective-permute-start.9 = (f32[64,128]{1,0:T(8,128)S(1)}, f32[64,128]{1,0:T(8,128)S(1)}, u32[]{:S(2)}, u32[]{:S(2)}) collective-permute-start(f32[64,128]{1,0:T(8,128)S(1)} %add_add_fusion.1), channel_id=1, source_target_pairs={{0,24},{8,16},{16,8},{24,0},{1,25},{9,17},{17,9},{25,1},{2,26},{10... | collective-permute-start | bytes 98312 | tf_op jit(solution)/shard_map/ppermute | solution.py:42
  194.2 5.1 %collective-permute-start.8 = (f32[64,128]{1,0:T(8,128)S(1)}, f32[64,128]{1,0:T(8,128)S(1)}, u32[]{:S(2)}, u32[]{:S(2)}) collective-permute-start(f32[64,128]{1,0:T(8,128)S(1)} %add_add_fusion.1), channel_id=1, source_target_pairs={{0,16},{8,24},{16,0},{24,8},{1,17},{9,25},{17,1},{25,9},{2,18},{10... | collective-permute-start | bytes 98312 | tf_op jit(solution)/shard_map/ppermute | solution.py:42
  194.4 5.0 %collective-permute-start.7 = (f32[64,128]{1,0:T(8,128)S(1)}, f32[64,128]{1,0:T(8,128)S(1)}, u32[]{:S(2)}, u32[]{:S(2)}) collective-permute-start(f32[64,128]{1,0:T(8,128)S(1)} %add_add_fusion.1), channel_id=1, source_target_pairs={{0,8},{8,0},{16,24},{24,16},{1,9},{9,1},{17,25},{25,17},{2,10},{10... | collective-permute-start | bytes 98312 | tf_op jit(solution)/shard_map/ppermute | solution.py:42
  211.3 5.1 %collective-permute-start.16 = (f32[64,64]{1,0:T(8,128)S(1)}, f32[64,64]{1,0:T(8,128)S(1)}, u32[]{:S(2)}, u32[]{:S(2)}) collective-permute-start(f32[64,64]{1,0:T(8,128)S(1)} %shard_map.66), channel_id=1, source_target_pairs={{0,7},{1,6},{2,5},{3,4},{4,3},{5,2},{6,1},{7,0},{8,15},{9,14},{10,... | collective-permute-start | bytes 49160 | tf_op jit(solution)/shard_map/ppermute | solution.py:42
  211.4 5.6 %collective-permute-start.15 = (f32[64,64]{1,0:T(8,128)S(1)}, f32[64,64]{1,0:T(8,128)S(1)}, u32[]{:S(2)}, u32[]{:S(2)}) collective-permute-start(f32[64,64]{1,0:T(8,128)S(1)} %shard_map.66), channel_id=1, source_target_pairs={{0,6},{1,7},{2,4},{3,5},{4,2},{5,3},{6,0},{7,1},{8,14},{9,15},{10,... | collective-permute-start | bytes 49160 | tf_op jit(solution)/shard_map/ppermute | solution.py:42
  213.4 10.5 %collective-permute-start.14 = (f32[64,64]{1,0:T(8,128)S(1)}, f32[64,64]{1,0:T(8,128)S(1)}, u32[]{:S(2)}, u32[]{:S(2)}) collective-permute-start(f32[64,64]{1,0:T(8,128)S(1)} %shard_map.66), channel_id=1, source_target_pairs={{0,5},{1,4},{2,7},{3,6},{4,1},{5,0},{6,3},{7,2},{8,13},{9,12},{10,... | collective-permute-start | bytes 49160 | tf_op jit(solution)/shard_map/ppermute | solution.py:42
  214.9 8.9 %collective-permute-start.13 = (f32[64,64]{1,0:T(8,128)S(1)}, f32[64,64]{1,0:T(8,128)S(1)}, u32[]{:S(2)}, u32[]{:S(2)}) collective-permute-start(f32[64,64]{1,0:T(8,128)S(1)} %shard_map.66), channel_id=1, source_target_pairs={{0,4},{1,5},{2,6},{3,7},{4,0},{5,1},{6,2},{7,3},{8,12},{9,13},{10,... | collective-permute-start | bytes 49160 | tf_op jit(solution)/shard_map/ppermute | solution.py:42
  216.4 7.5 %collective-permute-start.12 = (f32[64,64]{1,0:T(8,128)S(1)}, f32[64,64]{1,0:T(8,128)S(1)}, u32[]{:S(2)}, u32[]{:S(2)}) collective-permute-start(f32[64,64]{1,0:T(8,128)S(1)} %shard_map.66), channel_id=1, source_target_pairs={{0,3},{1,2},{2,1},{3,0},{4,7},{5,6},{6,5},{7,4},{8,11},{9,10},{10,... | collective-permute-start | bytes 49160 | tf_op jit(solution)/shard_map/ppermute | solution.py:42
  216.4 7.5 %collective-permute-start.11 = (f32[64,64]{1,0:T(8,128)S(1)}, f32[64,64]{1,0:T(8,128)S(1)}, u32[]{:S(2)}, u32[]{:S(2)}) collective-permute-start(f32[64,64]{1,0:T(8,128)S(1)} %shard_map.66), channel_id=1, source_target_pairs={{0,2},{1,3},{2,0},{3,1},{4,6},{5,7},{6,4},{7,5},{8,10},{9,11},{10,... | collective-permute-start | bytes 49160 | tf_op jit(solution)/shard_map/ppermute | solution.py:42
  217.0 6.9 %collective-permute-start.10 = (f32[64,64]{1,0:T(8,128)S(1)}, f32[64,64]{1,0:T(8,128)S(1)}, u32[]{:S(2)}, u32[]{:S(2)}) collective-permute-start(f32[64,64]{1,0:T(8,128)S(1)} %shard_map.66), channel_id=1, source_target_pairs={{0,1},{1,0},{2,3},{3,2},{4,5},{5,4},{6,7},{7,6},{8,9},{9,8},{10,11... | collective-permute-start | bytes 49160 | tf_op jit(solution)/shard_map/ppermute | solution.py:42
  223.9 5.9 %collective-permute-start.19 = (f32[64,64]{1,0:T(8,128)S(1)}, f32[64,64]{1,0:T(8,128)S(1)}, u32[]{:S(2)}, u32[]{:S(2)}) collective-permute-start(f32[64,64]{1,0:T(8,128)S(1)} %add_add_fusion), channel_id=1, source_target_pairs={{0,24},{8,16},{16,8},{24,0},{1,25},{9,17},{17,9},{25,1},{2,26},{10... | collective-permute-start | bytes 49160 | tf_op jit(solution)/shard_map/ppermute | solution.py:42
  226.0 4.9 %collective-permute-start.18 = (f32[64,64]{1,0:T(8,128)S(1)}, f32[64,64]{1,0:T(8,128)S(1)}, u32[]{:S(2)}, u32[]{:S(2)}) collective-permute-start(f32[64,64]{1,0:T(8,128)S(1)} %add_add_fusion), channel_id=1, source_target_pairs={{0,16},{8,24},{16,0},{24,8},{1,17},{9,25},{17,1},{25,9},{2,18},{10... | collective-permute-start | bytes 49160 | tf_op jit(solution)/shard_map/ppermute | solution.py:42
  227.1 4.1 %collective-permute-start.17 = (f32[64,64]{1,0:T(8,128)S(1)}, f32[64,64]{1,0:T(8,128)S(1)}, u32[]{:S(2)}, u32[]{:S(2)}) collective-permute-start(f32[64,64]{1,0:T(8,128)S(1)} %add_add_fusion), channel_id=1, source_target_pairs={{0,8},{8,0},{16,24},{24,16},{1,9},{9,1},{17,25},{25,17},{2,10},{10... | collective-permute-start | bytes 49160 | tf_op jit(solution)/shard_map/ppermute | solution.py:42
  231.8 1.3 copy-start.15

commit v3 on v1

v3 whole, which is shorter than its diff:
```python
import functools

import jax
import jax.numpy as jnp
from jax import lax
from jax.experimental import pallas as pl
from jax.experimental.pallas import tpu as pltpu
from jax.sharding import PartitionSpec as P

CENTER = 1.0
HALF_WIDTH = 0.5
HIGHEST = lax.Precision.HIGHEST
NT = (((1,), (1,)), ((), ()))
NN = (((1,), (0,)), ((), ()))
BF16 = jnp.bfloat16
F32 = jnp.float32
VMEM = pl.BlockSpec(memory_space=pltpu.VMEM)
SMEM = pl.BlockSpec(memory_space=pltpu.SMEM)
DEGREE_ROWS = 16


def call(kernel, out_shape, scratch, limit, args, flops=0, smem=0):
    moved = sum(x.size * x.dtype.itemsize for x in args)
    return pl.pallas_call(
        kernel,
        out_shape=out_shape,
        in_specs=[SMEM] * smem + [VMEM] * (len(args) - smem),
        out_specs=jax.tree.map(lambda _: VMEM, out_shape),
        scratch_shapes=scratch,
        compiler_params=pltpu.CompilerParams(vmem_limit_bytes=limit * 2**20),
        cost_estimate=pl.CostEstimate(flops=flops, bytes_accessed=moved, transcendentals=0),
    )(*args)


def trade(part, axis, d):
    n = lax.axis_size(axis)
    return lax.ppermute(part, axis, [(i, i ^ d) for i in range(n)])


def exchange(parts, axis, step=1):
    return [trade(part, axis, step * d) for d, part in enumerate(parts, 1)]


def tiles_first(ref, width):
    return [ref[:, k * width : (k + 1) * width] for k in range(ref.shape[1] // width)]


def round_kernel(vec_ref, out_ref):
    for k, piece in enumerate(tiles_first(vec_ref, out_ref.shape[2])):
        out_ref[k] = piece.astype(BF16)


def split_degree(sums, height):
    high = sums.astype(BF16).astype(F32)
    low = (sums - high).astype(BF16).astype(F32)
    rest = sums - high - low
    pad = jnp.zeros((height - 3 * sums.shape[0], sums.shape[1]), F32)
    return jnp.concatenate([high, low, rest, pad], 0).astype(BF16)


def join_degree(block, group):
    block = block.astype(F32)
    return (block[2 * group : 3 * group] + block[group : 2 * group]) + block[:group]


def degree_of(total, start, group, vectors_n):
    return jnp.concatenate(
        [total[start + k, vectors_n : vectors_n + 1, :] for k in range(group)], 0
    )


def place(tile, group, me, halves):
    apart = (tile // group) ^ me
    if halves:
        apart = (apart % 2) * halves + apart // 2
    return apart * group + tile % group


def product_kernel(parts_n, degree, dims, halves, meta, in_rows, out_rows, tiles_ref, *refs):
    part_refs, refs = refs[:parts_n], refs[parts_n:]
    own_ref, send_refs, (panel, total) = refs[0], refs[1:-2], refs[-2:]
    group, vectors_n, width = own_ref.shape[-3], part_refs[0].shape[-2], own_ref.shape[-1]
    place_at = 0
    for part in part_refs:
        blocks = part.reshape(-1, vectors_n, width)
        count = blocks.shape[0]
        panel[place_at : place_at + count, :vectors_n, :] = blocks[...]
        place_at += count
    if degree:
        panel[:, vectors_n:, :] = jnp.ones(
            (panel.shape[0], panel.shape[1] - vectors_n, width), BF16
        )
    total[...] = jnp.zeros_like(total)
    for t in range(tiles_ref.shape[0]):
        source = place(in_rows[t], group, meta[0], halves[0])
        target = place(out_rows[t], group, meta[1], halves[1])
        total[target] += lax.dot_general(
            panel[source], tiles_ref[t], dims, preferred_element_type=F32
        )
    kept = 1
    if halves[1]:
        kept = halves[1]
        for d in range(kept):
            own_ref[d] = total[d * group : (d + 1) * group]
        sends = [send_refs[0].at[d] for d in range(kept)]
    else:
        own_ref[...] = total[:group]
        sends = send_refs
    for d, send in enumerate(sends, kept):
        send[:group] = total[d * group : (d + 1) * group, :vectors_n, :].astype(BF16)
        if degree:
            send[group] = split_degree(degree_of(total, d * group, group, vectors_n), vectors_n)


def products(tiles, in_rows, out_rows, meta, parts, group, out_n, dims, halves, degree):
    vectors_n, width = parts[0].shape[-2:]
    height = vectors_n + (DEGREE_ROWS if degree else 0)
    blocks = group + (1 if degree else 0)
    half = halves[1]
    if half:
        out_shape = [
            jax.ShapeDtypeStruct((half, group, height, width), F32),
            jax.ShapeDtypeStruct((half, blocks, vectors_n, width), BF16),
        ]
    else:
        out_shape = [jax.ShapeDtypeStruct((group, height, width), F32)]
        out_shape += [jax.ShapeDtypeStruct((blocks, vectors_n, width), BF16)] * (out_n - 1)
    in_blocks = sum(part.size for part in parts) // (vectors_n * width)
    scratch = [
        pltpu.VMEM((in_blocks, height, width), BF16),
        pltpu.VMEM((out_n * group, height, width), F32),
    ]
    kernel = functools.partial(product_kernel, len(parts), degree, dims, halves)
    flops = 2 * tiles.size * height
    args = [meta, in_rows, out_rows, tiles, *parts]
    own, *send = call(kernel, out_shape, scratch, 24, args, flops, 3)
    return own, send


def merge_kernel(degree, kept, got, own_ref, *send_refs):
    _, group, height, width = kept.shape
    vectors_n = got.shape[2]
    for k in range(group):
        own_ref[k, :vectors_n, :] = kept[0, k, :vectors_n, :] + got[0, k].astype(F32)
        for d, send in enumerate(send_refs, 1):
            send[k] = (kept[d, k, :vectors_n, :] + got[d, k].astype(F32)).astype(BF16)
    if degree:
        sums = [
            degree_of(kept.at[d], 0, group, vectors_n) + join_degree(got[d, group], group)
            for d in range(kept.shape[0])
        ]
        for k in range(group):
            own_ref[k, vectors_n:, :] = jnp.broadcast_to(
                sums[0][k : k + 1], (height - vectors_n, width)
            )
        for d, send in enumerate(send_refs, 1):
            send[group] = split_degree(sums[d], vectors_n)


def merge(kept, got, degree):
    out_shape = [jax.ShapeDtypeStruct(kept.shape[1:], F32)]
    out_shape += [jax.ShapeDtypeStruct(got.shape[1:], BF16)] * (kept.shape[0] - 1)
    own, *send = call(functools.partial(merge_kernel, degree), out_shape, [], 24, [kept, got])
    return own, send


def gathered_sum(own, received, k, rows):
    total = own[k, rows, :]
    for part in received:
        total = total + part[k, rows, :].astype(F32)
    return total


def first_kernel(rows_n, chips_n, vec_ref, row_own, col_own, *refs):
    row_refs, refs = refs[: chips_n - 1], refs[chips_n - 1 :]
    col_refs, refs = refs[: rows_n - 1], refs[rows_n - 1 :]
    first_ref, rounded_ref, degree_ref = refs
    group, vectors_n, width = rounded_ref.shape
    degree = jnp.zeros((group, width), F32)
    for own, received in ((row_own, row_refs), (col_own, col_refs)):
        degree += degree_of(own, 0, group, vectors_n)
        for part in received:
            degree += join_degree(part[group], group)
    degree = 0.5 * degree
    degree_ref[...] = degree
    every = slice(0, vectors_n)
    for k, vec in enumerate(tiles_first(vec_ref, width)):
        symmetric = 0.5 * (
            gathered_sum(row_own, row_refs, k, every) + gathered_sum(col_own, col_refs, k, every)
        )
        image = degree[k : k + 1, :] * vec - symmetric
        first = (image - CENTER * vec) / HALF_WIDTH
        first_ref[:, k * width : (k + 1) * width] = first
        rounded_ref[k] = first.astype(BF16)


def filter_kernel(rows_n, chips_n, start_ref, first_ref, degree_ref, row_own, col_own, *refs):
    row_refs, refs = refs[: chips_n - 1], refs[chips_n - 1 :]
    col_refs, refs = refs[: rows_n - 1], refs[rows_n - 1 :]
    filtered_ref, rounded_ref, gram_ref, both = refs
    group, vectors_n, width = rounded_ref.shape
    every = slice(0, vectors_n)
    for k, vec in enumerate(tiles_first(first_ref, width)):
        symmetric = 0.5 * (
            gathered_sum(row_own, row_refs, k, every) + gathered_sum(col_own, col_refs, k, every)
        )
        columns = slice(k * width, (k + 1) * width)
        image = degree_ref[k : k + 1, :] * vec - symmetric
        filtered = 2.0 * (image - CENTER * vec) / HALF_WIDTH - start_ref[:, columns]
        filtered_ref[:, columns] = filtered
        rounded_ref[k] = filtered.astype(BF16)
        both[:vectors_n, columns] = filtered
        both[vectors_n:, columns] = degree_ref[k : k + 1, :] * filtered
    gram_ref[...] = lax.dot_general(
        filtered_ref[...], both[...], NT, precision=HIGHEST, preferred_element_type=F32
    )


def form_kernel(parts_n, halves, meta, tile_rows, tile_cols, tiles_ref, gram_ref, *refs):
    part_refs, (out_ref, panel, left, right) = refs[:parts_n], refs[parts_n:]
    group, (_, vectors_n, width) = part_refs[-1].shape[0], panel.shape
    place_at = 0
    for part in part_refs:
        blocks = part.reshape(-1, vectors_n, width)
        panel[place_at : place_at + blocks.shape[0]] = blocks[...]
        place_at += blocks.shape[0]
    cols_at = 2 * halves * group
    for t in range(tiles_ref.shape[0]):
        row = place(tile_rows[t], group, meta[1], halves)
        col = place(tile_cols[t], group, meta[0], 0) + cols_at
        columns = slice(t * width, (t + 1) * width)
        left[:, columns] = panel[row]
        right[:, columns] = lax.dot_general(
            panel[col], tiles_ref[t], NT, preferred_element_type=F32
        ).astype(BF16)
    form = lax.dot_general(left[...], right[...], NT, preferred_element_type=F32)
    out_ref[...] = jnp.concatenate([gram_ref[...], form], 1)


def all_sum(part):
    for axis in ("col", "row"):
        d = 1
        while d < lax.axis_size(axis):
            part = part + trade(part, axis, d)
            d *= 2
    return part


def local(tiles, tile_rows, tile_cols, start):
    tiles, tile_rows, tile_cols = tiles[0, 0], tile_rows[0, 0], tile_cols[0, 0]
    width = tiles.shape[-1]
    vectors_n, own_nodes = start.shape
    rows_n, cols_n = lax.axis_size("row"), lax.axis_size("col")
    total_nodes = own_nodes * rows_n * cols_n
    group = own_nodes // width
    row_me, col_me = lax.axis_index("row"), lax.axis_index("col")
    meta = jnp.stack([row_me, col_me]).astype(jnp.int32)
    swapped = jnp.stack([col_me, row_me]).astype(jnp.int32)

    rounded_shape = jax.ShapeDtypeStruct((group, vectors_n, width), BF16)
    vector_shape = jax.ShapeDtypeStruct((vectors_n, own_nodes), F32)

    chips_n = cols_n // 2

    def gather(rounded):
        chips = jnp.stack([rounded, *exchange([rounded] * (chips_n - 1), "col", 2)])
        col_parts = [rounded, *exchange([rounded] * (rows_n - 1), "row")]
        return col_parts, [chips, trade(chips, "col", 1)]

    def apply(rounded, degree):
        col_parts, row_parts = gather(rounded)
        col_own, col_send = products(
            tiles, tile_rows, tile_cols, swapped, row_parts, group, rows_n, NN, (chips_n, 0), degree
        )
        col_got = exchange(col_send, "row")
        kept, (send,) = products(
            tiles, tile_cols, tile_rows, meta, col_parts, group, cols_n, NT, (0, chips_n), degree
        )
        row_own, row_send = merge(kept, trade(send, "col", 1), degree)
        row_got = exchange(row_send, "col", 2)
        return [row_own, col_own, *row_got, *col_got]

    rounded = call(round_kernel, rounded_shape, [], 16, [start])
    sums = apply(rounded, True)
    first, rounded, degree = call(
        functools.partial(first_kernel, rows_n, chips_n),
        [vector_shape, rounded_shape, jax.ShapeDtypeStruct((group, width), F32)],
        [],
        24,
        [start, *sums],
    )
    sums = apply(rounded, False)
    filtered, rounded, gram = call(
        functools.partial(filter_kernel, rows_n, chips_n),
        [vector_shape, rounded_shape, jax.ShapeDtypeStruct((vectors_n, 2 * vectors_n), F32)],
        [pltpu.VMEM((2 * vectors_n, own_nodes), F32)],
        24,
        [start, first, degree, *sums],
    )
    col_parts, row_parts = gather(rounded)
    parts = [*row_parts, *col_parts]
    spread = (vectors_n, tiles.shape[0] * width)
    form = call(
        functools.partial(form_kernel, len(parts), chips_n),
        jax.ShapeDtypeStruct((vectors_n, 3 * vectors_n), F32),
        [
            pltpu.VMEM(((cols_n + rows_n) * group, vectors_n, width), BF16),
            pltpu.VMEM(spread, BF16),
            pltpu.VMEM(spread, BF16),
        ],
        24,
        [meta, tile_rows, tile_cols, tiles, gram, *parts],
        2 * tiles.size * vectors_n,
        3,
    )
    sums = all_sum(form) / total_nodes
    gram, scaled, form = (sums[:, i * vectors_n : (i + 1) * vectors_n] for i in range(3))
    factor = jnp.linalg.cholesky(gram)
    inverse = jax.scipy.linalg.solve_triangular(
        factor, jnp.eye(vectors_n, dtype=F32), lower=True
    )
    projected = scaled - 0.5 * (form + form.T)
    rayleigh = jnp.dot(
        jnp.dot(inverse, projected, precision=HIGHEST), inverse.T, precision=HIGHEST
    )
    ritz = jnp.dot(
        jnp.dot(rayleigh.T, inverse, precision=HIGHEST), filtered, precision=HIGHEST
    )
    return (ritz, rayleigh)


def solution(mesh):
    placed = (
        P("row", "col", None, None, None),
        P("row", "col", None),
        P("row", "col", None),
        P(None, ("row", "col")),
    )
    return jax.shard_map(
        local, mesh=mesh, in_specs=placed, out_specs=(P(None, ("row", "col")), P()), check_vma=False
    )
```

time: 170 us -> 140 us (0.82)
  starting transfers between devices: 85.8 us -> 56.9 us
  waiting for transfers between devices: 52.2 us -> 56.9 us
  Pallas kernels: 12.9 us -> 9.17 us
  local copies, waits for them, and re-layouts: 3.35 us -> 1.12 us
    ppermute x70 -> x40, starting transfers between devices: 85.8 us -> 56.9 us  [trade(): return lax.ppermute(part, axis, [(i, i ^ d) for i in range(n)])]
    ppermute x70 -> x40, waiting for transfers between devices: 52.2 us -> 56.9 us  [trade(): return lax.ppermute(part, axis, [(i, i ^ d) for i in range(n)])]
    pallas_call x8 -> x10, Pallas kernels: 12.9 us -> 9.17 us  [call(): pl.pallas_call(kernel, out_shape=out_shape, in_specs=[SMEM] * smem + [VME...]
    unnamed x14 -> x12, local copies, waits for them, and re-layouts: 3.21 us -> 0.97 us
    another operation x3 -> x6, other arithmetic: 6.51 us -> 6.72 us  [the longest x3 6.52 us: local(): factor = jnp.linalg.cholesky(gram)]
  transfers between devices with their start and end apart: 70 -> 40, of which waited for: 25 -> 18; matrix products, arithmetic and copies ran while one was open for 7% -> 0% of each run, Pallas kernels for 3% -> 5%
where the time goes in v3:
time: 140 us
  starting transfers between devices  56.9 us (41%)
  waiting for transfers between devices  56.9 us (41%)
  other arithmetic  12.5 us (9%)
  Pallas kernels  9.17 us (7%)
  matrix products  1.95 us (1%)
    ppermute x40, starting transfers between devices, trade(): return lax.ppermute(part, axis, [(i, i ^ d) for i in range(n)])  56.9 us
    ppermute x40, waiting for transfers between devices, trade(): return lax.ppermute(part, axis, [(i, i ^ d) for i in range(n)])  56.9 us
    pallas_call x10, Pallas kernels, call(): pl.pallas_call(kernel, out_shape=out_shape, in_specs=[SMEM] * smem + [VME...  9.17 us
    another operation x3, other arithmetic, local(): factor = jnp.linalg.cholesky(gram)  6.52 us
    another operation x2, other arithmetic, local(): jax.scipy.linalg.solve_triangular(factor, jnp.eye(vectors_n, dtype=F32),...  5.55 us
  transfers between devices with their start and end apart: 40, of which 18 were waited for; matrix products, arithmetic and copies ran while one was open for 0% of the time, Pallas kernels for 5%

profile of v3, /device:TPU:0, one launch (start us, length us, event | category | flops | bytes accessed | tf_op | source)
XLA Modules:
  0.0 139.5 jit_solution(12633983496444347120)
XLA Ops:
  1.6 4.0 %collective-permute-start.6 = (bf16[8,64,128]{2,1,0:T(8,128)(2,1)S(1)}, bf16[8,64,128]{2,1,0:T(8,128)(2,1)S(1)}, u32[]{:S(2)}, u32[]{:S(2)}) collective-permute-start(bf16[8,64,128]{2,1,0:T(8,128)(2,1)S(1)} %shard_map.59.refs_0_), channel_id=1, source_target_pairs={{0,6},{1,7},{2,4},{3,5},{4,2},{5,3},{6,0},{7,1},{8,14},{9,15},{10,... | collective-permute-start | bytes 393224 | tf_op jit(solution)/shard_map/ppermute | solution.py:37
  6.2 2.0 %collective-permute-start = (bf16[8,64,128]{2,1,0:T(8,128)(2,1)S(1)}, bf16[8,64,128]{2,1,0:T(8,128)(2,1)S(1)}, u32[]{:S(2)}, u32[]{:S(2)}) collective-permute-start(bf16[8,64,128]{2,1,0:T(8,128)(2,1)S(1)} %shard_map.59.refs_0_), channel_id=1, source_target_pairs={{0,8},{8,0},{16,24},{24,16},{1,9},{9,1},{17,25},{25,17},{2,10},{10... | collective-permute-start | bytes 393224 | tf_op jit(solution)/shard_map/ppermute | solution.py:37
  8.2 2.6 %collective-permute-start.1 = (bf16[8,64,128]{2,1,0:T(8,128)(2,1)S(1)}, bf16[8,64,128]{2,1,0:T(8,128)(2,1)S(1)}, u32[]{:S(2)}, u32[]{:S(2)}) collective-permute-start(bf16[8,64,128]{2,1,0:T(8,128)(2,1)S(1)} %shard_map.59.refs_0_), channel_id=1, source_target_pairs={{0,16},{8,24},{16,0},{24,8},{1,17},{9,25},{17,1},{25,9},{2,18},{10... | collective-permute-start | bytes 393224 | tf_op jit(solution)/shard_map/ppermute | solution.py:37
  10.8 2.4 %collective-permute-start.2 = (bf16[8,64,128]{2,1,0:T(8,128)(2,1)S(1)}, bf16[8,64,128]{2,1,0:T(8,128)(2,1)S(1)}, u32[]{:S(2)}, u32[]{:S(2)}) collective-permute-start(bf16[8,64,128]{2,1,0:T(8,128)(2,1)S(1)} %shard_map.59.refs_0_), channel_id=1, source_target_pairs={{0,24},{8,16},{16,8},{24,0},{1,25},{9,17},{17,9},{25,1},{2,26},{10... | collective-permute-start | bytes 393224 | tf_op jit(solution)/shard_map/ppermute | solution.py:37
  13.4 6.9 %collective-permute-done.1.refs_2_ = bf16[8,64,128]{2,1,0:T(8,128)(2,1)S(1)} collective-permute-done((bf16[8,64,128]{2,1,0:T(8,128)(2,1)S(1)}, bf16[8,64,128]{2,1,0:T(8,128)(2,1)S(1)}, u32[]{:S(2)}, u32[]{:S(2)}) %collective-permute-start.1) | collective-permute-done | bytes 131104 | tf_op jit(solution)/shard_map/ppermute | solution.py:37
  20.3 1.8 %shard_map.60 = (f32[4,8,80,128]{3,2,1,0:T(8,128)S(1)}, bf16[4,9,64,128]{3,2,1,0:T(8,128)(2,1)S(1)}) custom-call(s32[2]{0:T(128)S(1)} %pad_add_fusion.meta, s32[32]{0:T(128)S(1)} %bitcast.53, s32[32]{0:T(128)S(1)} %bitcast.48, bf16[32,128,128]{2,1,0:T(8,128)(2,1)S(1)} %bitcast.40, bf16[8,64,128]{2,1,0:T(8,128)(2,1)S(1)} %shard_map.59.refs_0_, ...), custom_call_target="tpu_custom_call" | custom-call | flops 83886080 | bytes 1573128 | tf_op jit(solution)/shard_map/pallas_call | solution.py:24
  22.3 1.5 %shard_map.62 = (f32[8,80,128]{2,1,0:T(8,128)S(1)}, bf16[9,64,128]{2,1,0:T(8,128)(2,1)S(1)}, bf16[9,64,128]{2,1,0:T(8,128)(2,1)S(1)}, bf16[9,64,128]{2,1,0:T(8,128)(2,1)S(1)}) custom-call(s32[2]{0:T(128)S(1)} %pad_add_fusion.1.meta, s32[32]{0:T(128)S(1)} %bitcast.49, s32[32]{0:T(128)S(1)} %bitcast.54, bf16[32,128,128]{2,1,0:T(8,128)(2,1)S(1)} %bitcast.41, ...), custom_call_target="tpu_custom_call" | custom-call | flops 83886080 | bytes 2097416 | tf_op jit(solution)/shard_map/pallas_call | solution.py:24
  23.8 2.0 %collective-permute-start.11 = (bf16[9,64,128]{2,1,0:T(8,128)(2,1)S(1)}, bf16[9,64,128]{2,1,0:T(8,128)(2,1)S(1)}, u32[]{:S(2)}, u32[]{:S(2)}) collective-permute-start(bf16[9,64,128]{2,1,0:T(8,128)(2,1)S(1)} %get-tuple-element.35), channel_id=1, source_target_pairs={{0,8},{8,0},{16,24},{24,16},{1,9},{9,1},{17,25},{25,17},{2,10},{10... | collective-permute-start | bytes 442376 | tf_op jit(solution)/shard_map/ppermute | solution.py:37
  25.8 1.1 collective-permute-start.12
  26.9 1.4 collective-permute-start.13
  28.4 1.6 %collective-permute-start.8 = (bf16[9,64,128]{2,1,0:T(8,128)(2,1)S(1)}, bf16[9,64,128]{2,1,0:T(8,128)(2,1)S(1)}, u32[]{:S(2)}, u32[]{:S(2)}) collective-permute-start(bf16[9,64,128]{2,1,0:T(8,128)(2,1)S(1)} %get-tuple-element.32), channel_id=1, source_target_pairs={{0,2},{1,3},{2,0},{3,1},{4,6},{5,7},{6,4},{7,5},{8,10},{9,11},{10,... | collective-permute-start | bytes 442376 | tf_op jit(solution)/shard_map/ppermute | solution.py:37
  30.0 1.5 %collective-permute-start.9 = (bf16[9,64,128]{2,1,0:T(8,128)(2,1)S(1)}, bf16[9,64,128]{2,1,0:T(8,128)(2,1)S(1)}, u32[]{:S(2)}, u32[]{:S(2)}) collective-permute-start(bf16[9,64,128]{2,1,0:T(8,128)(2,1)S(1)} %get-tuple-element.33), channel_id=1, source_target_pairs={{0,4},{1,5},{2,6},{3,7},{4,0},{5,1},{6,2},{7,3},{8,12},{9,13},{10,... | collective-permute-start | bytes 442376 | tf_op jit(solution)/shard_map/ppermute | solution.py:37
  31.5 1.6 %collective-permute-done.11.refs_3_ = bf16[9,64,128]{2,1,0:T(8,128)(2,1)S(1)} collective-permute-done((bf16[9,64,128]{2,1,0:T(8,128)(2,1)S(1)}, bf16[9,64,128]{2,1,0:T(8,128)(2,1)S(1)}, u32[]{:S(2)}, u32[]{:S(2)}) %collective-permute-start.11) | collective-permute-done | bytes 147488 | tf_op jit(solution)/shard_map/ppermute | solution.py:37
  33.1 2.4 %collective-permute-start.10 = (bf16[9,64,128]{2,1,0:T(8,128)(2,1)S(1)}, bf16[9,64,128]{2,1,0:T(8,128)(2,1)S(1)}, u32[]{:S(2)}, u32[]{:S(2)}) collective-permute-start(bf16[9,64,128]{2,1,0:T(8,128)(2,1)S(1)} %get-tuple-element.34), channel_id=1, source_target_pairs={{0,6},{1,7},{2,4},{3,5},{4,2},{5,3},{6,0},{7,1},{8,14},{9,15},{10,... | collective-permute-start | bytes 442376 | tf_op jit(solution)/shard_map/ppermute | solution.py:37
  35.5 4.3 %collective-permute-done.12.refs_4_ = bf16[9,64,128]{2,1,0:T(8,128)(2,1)S(1)} collective-permute-done((bf16[9,64,128]{2,1,0:T(8,128)(2,1)S(1)}, bf16[9,64,128]{2,1,0:T(8,128)(2,1)S(1)}, u32[]{:S(2)}, u32[]{:S(2)}) %collective-permute-start.12) | collective-permute-done | bytes 147488 | tf_op jit(solution)/shard_map/ppermute | solution.py:37
  40.0 3.1 %collective-permute-start.14 = (bf16[8,64,128]{2,1,0:T(8,128)(2,1)S(1)}, bf16[8,64,128]{2,1,0:T(8,128)(2,1)S(1)}, u32[]{:S(2)}, u32[]{:S(2)}) collective-permute-start(bf16[8,64,128]{2,1,0:T(8,128)(2,1)S(1)} %get-tuple-element.40.refs_0_), channel_id=1, source_target_pairs={{0,8},{8,0},{16,24},{24,16},{1,9},{9,1},{17,25},{25,17},{2,10},{10... | collective-permute-start | bytes 393224 | tf_op jit(solution)/shard_map/ppermute | solution.py:37
  44.2 1.4 collective-permute-start.16
  45.5 2.5 %collective-permute-start.20 = (bf16[8,64,128]{2,1,0:T(8,128)(2,1)S(1)}, bf16[8,64,128]{2,1,0:T(8,128)(2,1)S(1)}, u32[]{:S(2)}, u32[]{:S(2)}) collective-permute-start(bf16[8,64,128]{2,1,0:T(8,128)(2,1)S(1)} %get-tuple-element.40.refs_0_), channel_id=1, source_target_pairs={{0,6},{1,7},{2,4},{3,5},{4,2},{5,3},{6,0},{7,1},{8,14},{9,15},{10,... | collective-permute-start | bytes 393224 | tf_op jit(solution)/shard_map/ppermute | solution.py:37
  49.0 6.5 %collective-permute-done.15.refs_2_ = bf16[8,64,128]{2,1,0:T(8,128)(2,1)S(1)} collective-permute-done((bf16[8,64,128]{2,1,0:T(8,128)(2,1)S(1)}, bf16[8,64,128]{2,1,0:T(8,128)(2,1)S(1)}, u32[]{:S(2)}, u32[]{:S(2)}) %collective-permute-start.15) | collective-permute-done | bytes 131104 | tf_op jit(solution)/shard_map/ppermute | solution.py:37
  55.6 1.5 %shard_map.64 = (f32[4,8,64,128]{3,2,1,0:T(8,128)S(1)}, bf16[4,8,64,128]{3,2,1,0:T(8,128)(2,1)S(1)}) custom-call(s32[2]{0:T(128)S(1)} %pad_add_fusion.meta, s32[32]{0:T(128)S(1)} %bitcast.55, s32[32]{0:T(128)S(1)} %bitcast.50, bf16[32,128,128]{2,1,0:T(8,128)(2,1)S(1)} %bitcast.42, bf16[8,64,128]{2,1,0:T(8,128)(2,1)S(1)} %get-tuple-element.40.refs_0_, ...), custom_call_target="tpu_custom_call" | custom-call | flops 67108864 | bytes 1573128 | tf_op jit(solution)/shard_map/pallas_call | solution.py:24
  57.8 1.2 collective-permute-done.17.got
  59.2 1.6 %collective-permute-start.22 = (bf16[8,64,128]{2,1,0:T(8,128)(2,1)S(1)}, bf16[8,64,128]{2,1,0:T(8,128)(2,1)S(1)}, u32[]{:S(2)}, u32[]{:S(2)}) collective-permute-start(bf16[8,64,128]{2,1,0:T(8,128)(2,1)S(1)} %get-tuple-element.45), channel_id=1, source_target_pairs={{0,2},{1,3},{2,0},{3,1},{4,6},{5,7},{6,4},{7,5},{8,10},{9,11},{10,... | collective-permute-start | bytes 393224 | tf_op jit(solution)/shard_map/ppermute | solution.py:37
  60.7 1.5 %collective-permute-start.23 = (bf16[8,64,128]{2,1,0:T(8,128)(2,1)S(1)}, bf16[8,64,128]{2,1,0:T(8,128)(2,1)S(1)}, u32[]{:S(2)}, u32[]{:S(2)}) collective-permute-start(bf16[8,64,128]{2,1,0:T(8,128)(2,1)S(1)} %get-tuple-element.46), channel_id=1, source_target_pairs={{0,4},{1,5},{2,6},{3,7},{4,0},{5,1},{6,2},{7,3},{8,12},{9,13},{10,... | collective-permute-start | bytes 393224 | tf_op jit(solution)/shard_map/ppermute | solution.py:37
  62.7 1.4 shard_map.66
  64.1 2.0 %collective-permute-start.25 = (bf16[8,64,128]{2,1,0:T(8,128)(2,1)S(1)}, bf16[8,64,128]{2,1,0:T(8,128)(2,1)S(1)}, u32[]{:S(2)}, u32[]{:S(2)}) collective-permute-start(bf16[8,64,128]{2,1,0:T(8,128)(2,1)S(1)} %get-tuple-element.48), channel_id=1, source_target_pairs={{0,8},{8,0},{16,24},{24,16},{1,9},{9,1},{17,25},{25,17},{2,10},{10... | collective-permute-start | bytes 393224 | tf_op jit(solution)/shard_map/ppermute | solution.py:37
  67.1 1.4 %collective-permute-start.27 = (bf16[8,64,128]{2,1,0:T(8,128)(2,1)S(1)}, bf16[8,64,128]{2,1,0:T(8,128)(2,1)S(1)}, u32[]{:S(2)}, u32[]{:S(2)}) collective-permute-start(bf16[8,64,128]{2,1,0:T(8,128)(2,1)S(1)} %get-tuple-element.50), channel_id=1, source_target_pairs={{0,24},{8,16},{16,8},{24,0},{1,25},{9,17},{17,9},{25,1},{2,26},{10... | collective-permute-start | bytes 393224 | tf_op jit(solution)/shard_map/ppermute | solution.py:37
  68.8 1.5 %collective-permute-done.25.refs_3_ = bf16[8,64,128]{2,1,0:T(8,128)(2,1)S(1)} collective-permute-done((bf16[8,64,128]{2,1,0:T(8,128)(2,1)S(1)}, bf16[8,64,128]{2,1,0:T(8,128)(2,1)S(1)}, u32[]{:S(2)}, u32[]{:S(2)}) %collective-permute-start.25) | collective-permute-done | bytes 131104 | tf_op jit(solution)/shard_map/ppermute | solution.py:37
  70.3 8.2 %collective-permute-done.26.refs_4_ = bf16[8,64,128]{2,1,0:T(8,128)(2,1)S(1)} collective-permute-done((bf16[8,64,128]{2,1,0:T(8,128)(2,1)S(1)}, bf16[8,64,128]{2,1,0:T(8,128)(2,1)S(1)}, u32[]{:S(2)}, u32[]{:S(2)}) %collective-permute-start.26) | collective-permute-done | bytes 131104 | tf_op jit(solution)/shard_map/ppermute | solution.py:37
  79.3 2.5 %collective-permute-start.30 = (bf16[8,64,128]{2,1,0:T(8,128)(2,1)S(1)}, bf16[8,64,128]{2,1,0:T(8,128)(2,1)S(1)}, u32[]{:S(2)}, u32[]{:S(2)}) collective-permute-start(bf16[8,64,128]{2,1,0:T(8,128)(2,1)S(1)} %get-tuple-element.52.refs_2_), channel_id=1, source_target_pairs={{0,6},{1,7},{2,4},{3,5},{4,2},{5,3},{6,0},{7,1},{8,14},{9,15},{10,... | collective-permute-start | bytes 393224 | tf_op jit(solution)/shard_map/ppermute | solution.py:37
  82.8 2.4 %collective-permute-done.30 = bf16[8,64,128]{2,1,0:T(8,128)(2,1)S(1)} collective-permute-done((bf16[8,64,128]{2,1,0:T(8,128)(2,1)S(1)}, bf16[8,64,128]{2,1,0:T(8,128)(2,1)S(1)}, u32[]{:S(2)}, u32[]{:S(2)}) %collective-permute-start.30) | collective-permute-done | bytes 131104 | tf_op jit(solution)/shard_map/ppermute | solution.py:37
  85.2 1.5 %collective-permute-done.29 = bf16[8,64,128]{2,1,0:T(8,128)(2,1)S(1)} collective-permute-done((bf16[8,64,128]{2,1,0:T(8,128)(2,1)S(1)}, bf16[8,64,128]{2,1,0:T(8,128)(2,1)S(1)}, u32[]{:S(2)}, u32[]{:S(2)}) %collective-permute-start.29) | collective-permute-done | bytes 131104 | tf_op jit(solution)/shard_map/ppermute | solution.py:37
  87.4 2.1 %collective-permute-start.32 = (bf16[8,64,128]{2,1,0:T(8,128)(2,1)S(1)}, bf16[8,64,128]{2,1,0:T(8,128)(2,1)S(1)}, u32[]{:S(2)}, u32[]{:S(2)}) collective-permute-start(bf16[8,64,128]{2,1,0:T(8,128)(2,1)S(1)} %get-tuple-element.52.refs_2_), channel_id=1, source_target_pairs={{0,8},{8,0},{16,24},{24,16},{1,9},{9,1},{17,25},{25,17},{2,10},{10... | collective-permute-start | bytes 393224 | tf_op jit(solution)/shard_map/ppermute | solution.py:37
  89.6 1.3 collective-permute-start.33
  90.9 1.4 collective-permute-start.34
  92.3 3.7 %collective-permute-done.32.refs_3_ = bf16[8,64,128]{2,1,0:T(8,128)(2,1)S(1)} collective-permute-done((bf16[8,64,128]{2,1,0:T(8,128)(2,1)S(1)}, bf16[8,64,128]{2,1,0:T(8,128)(2,1)S(1)}, u32[]{:S(2)}, u32[]{:S(2)}) %collective-permute-start.32) | collective-permute-done | bytes 131104 | tf_op jit(solution)/shard_map/ppermute | solution.py:37
  95.9 6.5 %collective-permute-done.33.refs_4_ = bf16[8,64,128]{2,1,0:T(8,128)(2,1)S(1)} collective-permute-done((bf16[8,64,128]{2,1,0:T(8,128)(2,1)S(1)}, bf16[8,64,128]{2,1,0:T(8,128)(2,1)S(1)}, u32[]{:S(2)}, u32[]{:S(2)}) %collective-permute-start.33) | collective-permute-done | bytes 131104 | tf_op jit(solution)/shard_map/ppermute | solution.py:37
  102.5 1.8 %shard_map.68 = f32[64,192]{1,0:T(8,128)S(1)} custom-call(s32[2]{0:T(128)S(1)} %pad_add_fusion.meta, s32[32]{0:T(128)S(1)} %bitcast.52, s32[32]{0:T(128)S(1)} %bitcast.57, bf16[32,128,128]{2,1,0:T(8,128)(2,1)S(1)} %bitcast.44, f32[64,128]{1,0:T(8,128)S(1)} %get-tuple-element.51.gram_ref, bf16[4,8,64,128]{3,2,1,0:T(8,128)(2,1)S(1)} %pad_maximum_fusion.2.refs_0_, ...), custom_call_target="tpu_custom_call" | custom-call | flops 67108864 | bytes 2654472 | tf_op jit(solution)/shard_map/pallas_call | solution.py:24
  104.3 1.2 collective-permute-done.35
  105.6 1.1 collective-permute-start.36
  106.7 3.2 %collective-permute-done.36 = f32[64,192]{1,0:T(8,128)S(1)} collective-permute-done((f32[64,192]{1,0:T(8,128)S(1)}, f32[64,192]{1,0:T(8,128)S(1)}, u32[]{:S(2)}, u32[]{:S(2)}) %collective-permute-start.36) | collective-permute-done | bytes 49184 | tf_op jit(solution)/shard_map/ppermute | solution.py:37
  109.9 1.4 %collective-permute-start.37 = (f32[64,192]{1,0:T(8,128)S(1)}, f32[64,192]{1,0:T(8,128)S(1)}, u32[]{:S(2)}, u32[]{:S(2)}) collective-permute-start(f32[64,192]{1,0:T(8,128)S(1)} %add.31), channel_id=1, source_target_pairs={{0,4},{1,5},{2,6},{3,7},{4,0},{5,1},{6,2},{7,3},{8,12},{9,13},{10,... | collective-permute-start | bytes 147464 | tf_op jit(solution)/shard_map/ppermute | solution.py:37
  111.4 2.9 %collective-permute-done.37 = f32[64,192]{1,0:T(8,128)S(1)} collective-permute-done((f32[64,192]{1,0:T(8,128)S(1)}, f32[64,192]{1,0:T(8,128)S(1)}, u32[]{:S(2)}, u32[]{:S(2)}) %collective-permute-start.37) | collective-permute-done | bytes 49184 | tf_op jit(solution)/shard_map/ppermute | solution.py:37
  114.3 2.7 %collective-permute-start.38 = (f32[64,192]{1,0:T(8,128)S(1)}, f32[64,192]{1,0:T(8,128)S(1)}, u32[]{:S(2)}, u32[]{:S(2)}) collective-permute-start(f32[64,192]{1,0:T(8,128)S(1)} %add.32), channel_id=1, source_target_pairs={{0,8},{8,0},{16,24},{24,16},{1,9},{9,1},{17,25},{25,17},{2,10},{10... | collective-permute-start | bytes 147464 | tf_op jit(solution)/shard_map/ppermute | solution.py:37
  117.0 2.2 %collective-permute-done.38 = f32[64,192]{1,0:T(8,128)S(1)} collective-permute-done((f32[64,192]{1,0:T(8,128)S(1)}, f32[64,192]{1,0:T(8,128)S(1)}, u32[]{:S(2)}, u32[]{:S(2)}) %collective-permute-start.38) | collective-permute-done | bytes 49184 | tf_op jit(solution)/shard_map/ppermute | solution.py:37
  119.2 3.8 %collective-permute-start.39 = (f32[64,192]{1,0:T(8,128)S(1)}, f32[64,192]{1,0:T(8,128)S(1)}, u32[]{:S(2)}, u32[]{:S(2)}) collective-permute-start(f32[64,192]{1,0:T(8,128)S(1)} %add.33), channel_id=1, source_target_pairs={{0,16},{8,24},{16,0},{24,8},{1,17},{9,25},{17,1},{25,9},{2,18},{10... | collective-permute-start | bytes 147464 | tf_op jit(solution)/shard_map/ppermute | solution.py:37
  123.0 2.3 %collective-permute-done.39 = f32[64,192]{1,0:T(8,128)S(1)} collective-permute-done((f32[64,192]{1,0:T(8,128)S(1)}, f32[64,192]{1,0:T(8,128)S(1)}, u32[]{:S(2)}, u32[]{:S(2)}) %collective-permute-start.39) | collective-permute-done | bytes 49184 | tf_op jit(solution)/shard_map/ppermute | solution.py:37
  125.4 5.8 %cholesky.17 = f32[64,64]{1,0:T(8,128)S(1)} custom-call(f32[64,64]{1,0:T(8,128)S(1)} %get-tuple-element.55), custom_call_target="Cholesky" | custom-call | tf_op jit(solution)/shard_map/jit(cholesky)/cholesky | solution.py:318
  132.5 4.9 %custom-call.7 = f32[1,64,64]{1,2,0:T(8,128)S(1)} custom-call(f32[1,64,64]{2,1,0:T(8,128)S(1)} %fusion), custom_call_target="InvertDiagBlocksLowerTriangular" | custom-call | tf_op jit(solution)/shard_map/jit(_solve_triangular)/triangular_solve | solution.py:319
  (78 shorter events, 13.1 us)
Async XLA Ops:
  0.6 1.0 copy-start.1
  1.6 18.7 %copy-start = (bf16[1,1,32,128,128]{4,3,2,1,0:T(8,128)(2,1)S(1)}, bf16[1,1,32,128,128]{4,3,2,1,0:T(8,128)(2,1)}, u32[]{:S(2)}) copy-start(bf16[1,1,32,128,128]{4,3,2,1,0:T(8,128)(2,1)} %param.4) | copy-start | bytes 3145732
  1.6 18.7 %copy-start.3 = (s32[1,1,32]{2,1,0:T(1,128)S(1)}, s32[1,1,32]{2,1,0:T(1,128)}, u32[]{:S(2)}) copy-start(s32[1,1,32]{2,1,0:T(1,128)} %param.5) | copy-start | bytes 388
  1.6 18.7 %copy-start.4 = (s32[1,1,32]{2,1,0:T(1,128)S(1)}, s32[1,1,32]{2,1,0:T(1,128)}, u32[]{:S(2)}) copy-start(s32[1,1,32]{2,1,0:T(1,128)} %param.6) | copy-start | bytes 388
  1.6 9.2 %collective-permute-start.6 = (bf16[8,64,128]{2,1,0:T(8,128)(2,1)S(1)}, bf16[8,64,128]{2,1,0:T(8,128)(2,1)S(1)}, u32[]{:S(2)}, u32[]{:S(2)}) collective-permute-start(bf16[8,64,128]{2,1,0:T(8,128)(2,1)S(1)} %shard_map.59.refs_0_), channel_id=1, source_target_pairs={{0,6},{1,7},{2,4},{3,5},{4,2},{5,3},{6,0},{7,1},{8,14},{9,15},{10,... | collective-permute-start | bytes 393224 | tf_op jit(solution)/shard_map/ppermute | solution.py:37
  5.6 7.6 %collective-permute-start.5 = (bf16[8,64,128]{2,1,0:T(8,128)(2,1)S(1)}, bf16[8,64,128]{2,1,0:T(8,128)(2,1)S(1)}, u32[]{:S(2)}, u32[]{:S(2)}) collective-permute-start(bf16[8,64,128]{2,1,0:T(8,128)(2,1)S(1)} %shard_map.59.refs_0_), channel_id=1, source_target_pairs={{0,4},{1,5},{2,6},{3,7},{4,0},{5,1},{6,2},{7,3},{8,12},{9,13},{10,... | collective-permute-start | bytes 393224 | tf_op jit(solution)/shard_map/ppermute | solution.py:37
  6.1 7.1 %collective-permute-start.4 = (bf16[8,64,128]{2,1,0:T(8,128)(2,1)S(1)}, bf16[8,64,128]{2,1,0:T(8,128)(2,1)S(1)}, u32[]{:S(2)}, u32[]{:S(2)}) collective-permute-start(bf16[8,64,128]{2,1,0:T(8,128)(2,1)S(1)} %shard_map.59.refs_0_), channel_id=1, source_target_pairs={{0,2},{1,3},{2,0},{3,1},{4,6},{5,7},{6,4},{7,5},{8,10},{9,11},{10,... | collective-permute-start | bytes 393224 | tf_op jit(solution)/shard_map/ppermute | solution.py:37
  6.2 7.2 %collective-permute-start = (bf16[8,64,128]{2,1,0:T(8,128)(2,1)S(1)}, bf16[8,64,128]{2,1,0:T(8,128)(2,1)S(1)}, u32[]{:S(2)}, u32[]{:S(2)}) collective-permute-start(bf16[8,64,128]{2,1,0:T(8,128)(2,1)S(1)} %shard_map.59.refs_0_), channel_id=1, source_target_pairs={{0,8},{8,0},{16,24},{24,16},{1,9},{9,1},{17,25},{25,17},{2,10},{10... | collective-permute-start | bytes 393224 | tf_op jit(solution)/shard_map/ppermute | solution.py:37
  8.2 12.1 %collective-permute-start.1 = (bf16[8,64,128]{2,1,0:T(8,128)(2,1)S(1)}, bf16[8,64,128]{2,1,0:T(8,128)(2,1)S(1)}, u32[]{:S(2)}, u32[]{:S(2)}) collective-permute-start(bf16[8,64,128]{2,1,0:T(8,128)(2,1)S(1)} %shard_map.59.refs_0_), channel_id=1, source_target_pairs={{0,16},{8,24},{16,0},{24,8},{1,17},{9,25},{17,1},{25,9},{2,18},{10... | collective-permute-start | bytes 393224 | tf_op jit(solution)/shard_map/ppermute | solution.py:37
  10.8 9.5 %collective-permute-start.2 = (bf16[8,64,128]{2,1,0:T(8,128)(2,1)S(1)}, bf16[8,64,128]{2,1,0:T(8,128)(2,1)S(1)}, u32[]{:S(2)}, u32[]{:S(2)}) collective-permute-start(bf16[8,64,128]{2,1,0:T(8,128)(2,1)S(1)} %shard_map.59.refs_0_), channel_id=1, source_target_pairs={{0,24},{8,16},{16,8},{24,0},{1,25},{9,17},{17,9},{25,1},{2,26},{10... | collective-permute-start | bytes 393224 | tf_op jit(solution)/shard_map/ppermute | solution.py:37
  13.3 9.0 %collective-permute-start.7 = (bf16[4,8,64,128]{3,2,1,0:T(8,128)(2,1)S(1)}, bf16[4,8,64,128]{3,2,1,0:T(8,128)(2,1)S(1)}, u32[]{:S(2)}, u32[]{:S(2)}) collective-permute-start(bf16[4,8,64,128]{3,2,1,0:T(8,128)(2,1)S(1)} %pad_maximum_fusion.refs_0_), channel_id=1, source_target_pairs={{0,1},{1,0},{2,3},{3,2},{4,5},{5,4},{6,7},{7,6},{8,9},{9,8},{10,11... | collective-permute-start | bytes 1572872 | tf_op jit(solution)/shard_map/ppermute | solution.py:37
  22.1 6.2 %collective-permute-start.3 = (bf16[4,9,64,128]{3,2,1,0:T(8,128)(2,1)S(1)}, bf16[4,9,64,128]{3,2,1,0:T(8,128)(2,1)S(1)}, u32[]{:S(2)}, u32[]{:S(2)}) collective-permute-start(bf16[4,9,64,128]{3,2,1,0:T(8,128)(2,1)S(1)} %get-tuple-element.29), channel_id=1, source_target_pairs={{0,1},{1,0},{2,3},{3,2},{4,5},{5,4},{6,7},{7,6},{8,9},{9,8},{10,11... | collective-permute-start | bytes 1769480 | tf_op jit(solution)/shard_map/ppermute | solution.py:37
  23.8 16.0 %copy-start.2 = (f32[64,1024]{1,0:T(8,128)S(1)}, f32[64,1024]{1,0:T(8,128)}, u32[]{:S(2)}) copy-start(f32[64,1024]{1,0:T(8,128)} %start_ref.1) | copy-start | bytes 786436
  23.8 9.3 %collective-permute-start.11 = (bf16[9,64,128]{2,1,0:T(8,128)(2,1)S(1)}, bf16[9,64,128]{2,1,0:T(8,128)(2,1)S(1)}, u32[]{:S(2)}, u32[]{:S(2)}) collective-permute-start(bf16[9,64,128]{2,1,0:T(8,128)(2,1)S(1)} %get-tuple-element.35), channel_id=1, source_target_pairs={{0,8},{8,0},{16,24},{24,16},{1,9},{9,1},{17,25},{25,17},{2,10},{10... | collective-permute-start | bytes 442376 | tf_op jit(solution)/shard_map/ppermute | solution.py:37
  25.8 13.9 %collective-permute-start.12 = (bf16[9,64,128]{2,1,0:T(8,128)(2,1)S(1)}, bf16[9,64,128]{2,1,0:T(8,128)(2,1)S(1)}, u32[]{:S(2)}, u32[]{:S(2)}) collective-permute-start(bf16[9,64,128]{2,1,0:T(8,128)(2,1)S(1)} %get-tuple-element.36), channel_id=1, source_target_pairs={{0,16},{8,24},{16,0},{24,8},{1,17},{9,25},{17,1},{25,9},{2,18},{10... | collective-permute-start | bytes 442376 | tf_op jit(solution)/shard_map/ppermute | solution.py:37
  26.9 12.9 %collective-permute-start.13 = (bf16[9,64,128]{2,1,0:T(8,128)(2,1)S(1)}, bf16[9,64,128]{2,1,0:T(8,128)(2,1)S(1)}, u32[]{:S(2)}, u32[]{:S(2)}) collective-permute-start(bf16[9,64,128]{2,1,0:T(8,128)(2,1)S(1)} %get-tuple-element.37), channel_id=1, source_target_pairs={{0,24},{8,16},{16,8},{24,0},{1,25},{9,17},{17,9},{25,1},{2,26},{10... | collective-permute-start | bytes 442376 | tf_op jit(solution)/shard_map/ppermute | solution.py:37
  28.4 11.4 %collective-permute-start.8 = (bf16[9,64,128]{2,1,0:T(8,128)(2,1)S(1)}, bf16[9,64,128]{2,1,0:T(8,128)(2,1)S(1)}, u32[]{:S(2)}, u32[]{:S(2)}) collective-permute-start(bf16[9,64,128]{2,1,0:T(8,128)(2,1)S(1)} %get-tuple-element.32), channel_id=1, source_target_pairs={{0,2},{1,3},{2,0},{3,1},{4,6},{5,7},{6,4},{7,5},{8,10},{9,11},{10,... | collective-permute-start | bytes 442376 | tf_op jit(solution)/shard_map/ppermute | solution.py:37
  30.0 9.8 %collective-permute-start.9 = (bf16[9,64,128]{2,1,0:T(8,128)(2,1)S(1)}, bf16[9,64,128]{2,1,0:T(8,128)(2,1)S(1)}, u32[]{:S(2)}, u32[]{:S(2)}) collective-permute-start(bf16[9,64,128]{2,1,0:T(8,128)(2,1)S(1)} %get-tuple-element.33), channel_id=1, source_target_pairs={{0,4},{1,5},{2,6},{3,7},{4,0},{5,1},{6,2},{7,3},{8,12},{9,13},{10,... | collective-permute-start | bytes 442376 | tf_op jit(solution)/shard_map/ppermute | solution.py:37
  33.1 6.7 %collective-permute-start.10 = (bf16[9,64,128]{2,1,0:T(8,128)(2,1)S(1)}, bf16[9,64,128]{2,1,0:T(8,128)(2,1)S(1)}, u32[]{:S(2)}, u32[]{:S(2)}) collective-permute-start(bf16[9,64,128]{2,1,0:T(8,128)(2,1)S(1)} %get-tuple-element.34), channel_id=1, source_target_pairs={{0,6},{1,7},{2,4},{3,5},{4,2},{5,3},{6,0},{7,1},{8,14},{9,15},{10,... | collective-permute-start | bytes 442376 | tf_op jit(solution)/shard_map/ppermute | solution.py:37
  40.0 8.5 %collective-permute-start.14 = (bf16[8,64,128]{2,1,0:T(8,128)(2,1)S(1)}, bf16[8,64,128]{2,1,0:T(8,128)(2,1)S(1)}, u32[]{:S(2)}, u32[]{:S(2)}) collective-permute-start(bf16[8,64,128]{2,1,0:T(8,128)(2,1)S(1)} %get-tuple-element.40.refs_0_), channel_id=1, source_target_pairs={{0,8},{8,0},{16,24},{24,16},{1,9},{9,1},{17,25},{25,17},{2,10},{10... | collective-permute-start | bytes 393224 | tf_op jit(solution)/shard_map/ppermute | solution.py:37
  43.1 12.5 %collective-permute-start.15 = (bf16[8,64,128]{2,1,0:T(8,128)(2,1)S(1)}, bf16[8,64,128]{2,1,0:T(8,128)(2,1)S(1)}, u32[]{:S(2)}, u32[]{:S(2)}) collective-permute-start(bf16[8,64,128]{2,1,0:T(8,128)(2,1)S(1)} %get-tuple-element.40.refs_0_), channel_id=1, source_target_pairs={{0,16},{8,24},{16,0},{24,8},{1,17},{9,25},{17,1},{25,9},{2,18},{10... | collective-permute-start | bytes 393224 | tf_op jit(solution)/shard_map/ppermute | solution.py:37
  44.2 11.4 %collective-permute-start.16 = (bf16[8,64,128]{2,1,0:T(8,128)(2,1)S(1)}, bf16[8,64,128]{2,1,0:T(8,128)(2,1)S(1)}, u32[]{:S(2)}, u32[]{:S(2)}) collective-permute-start(bf16[8,64,128]{2,1,0:T(8,128)(2,1)S(1)} %get-tuple-element.40.refs_0_), channel_id=1, source_target_pairs={{0,24},{8,16},{16,8},{24,0},{1,25},{9,17},{17,9},{25,1},{2,26},{10... | collective-permute-start | bytes 393224 | tf_op jit(solution)/shard_map/ppermute | solution.py:37
  45.5 11.6 %collective-permute-start.20 = (bf16[8,64,128]{2,1,0:T(8,128)(2,1)S(1)}, bf16[8,64,128]{2,1,0:T(8,128)(2,1)S(1)}, u32[]{:S(2)}, u32[]{:S(2)}) collective-permute-start(bf16[8,64,128]{2,1,0:T(8,128)(2,1)S(1)} %get-tuple-element.40.refs_0_), channel_id=1, source_target_pairs={{0,6},{1,7},{2,4},{3,5},{4,2},{5,3},{6,0},{7,1},{8,14},{9,15},{10,... | collective-permute-start | bytes 393224 | tf_op jit(solution)/shard_map/ppermute | solution.py:37
  48.0 9.2 %collective-permute-start.19 = (bf16[8,64,128]{2,1,0:T(8,128)(2,1)S(1)}, bf16[8,64,128]{2,1,0:T(8,128)(2,1)S(1)}, u32[]{:S(2)}, u32[]{:S(2)}) collective-permute-start(bf16[8,64,128]{2,1,0:T(8,128)(2,1)S(1)} %get-tuple-element.40.refs_0_), channel_id=1, source_target_pairs={{0,4},{1,5},{2,6},{3,7},{4,0},{5,1},{6,2},{7,3},{8,12},{9,13},{10,... | collective-permute-start | bytes 393224 | tf_op jit(solution)/shard_map/ppermute | solution.py:37
  48.5 8.7 %collective-permute-start.18 = (bf16[8,64,128]{2,1,0:T(8,128)(2,1)S(1)}, bf16[8,64,128]{2,1,0:T(8,128)(2,1)S(1)}, u32[]{:S(2)}, u32[]{:S(2)}) collective-permute-start(bf16[8,64,128]{2,1,0:T(8,128)(2,1)S(1)} %get-tuple-element.40.refs_0_), channel_id=1, source_target_pairs={{0,2},{1,3},{2,0},{3,1},{4,6},{5,7},{6,4},{7,5},{8,10},{9,11},{10,... | collective-permute-start | bytes 393224 | tf_op jit(solution)/shard_map/ppermute | solution.py:37
  57.1 2.0 %collective-permute-start.17 = (bf16[4,8,64,128]{3,2,1,0:T(8,128)(2,1)S(1)}, bf16[4,8,64,128]{3,2,1,0:T(8,128)(2,1)S(1)}, u32[]{:S(2)}, u32[]{:S(2)}) collective-permute-start(bf16[4,8,64,128]{3,2,1,0:T(8,128)(2,1)S(1)} %get-tuple-element.42), channel_id=1, source_target_pairs={{0,1},{1,0},{2,3},{3,2},{4,5},{5,4},{6,7},{7,6},{8,9},{9,8},{10,11... | collective-permute-start | bytes 1572872 | tf_op jit(solution)/shard_map/ppermute | solution.py:37
  57.3 5.5 %collective-permute-start.21 = (bf16[4,8,64,128]{3,2,1,0:T(8,128)(2,1)S(1)}, bf16[4,8,64,128]{3,2,1,0:T(8,128)(2,1)S(1)}, u32[]{:S(2)}, u32[]{:S(2)}) collective-permute-start(bf16[4,8,64,128]{3,2,1,0:T(8,128)(2,1)S(1)} %pad_maximum_fusion.1.refs_0_), channel_id=1, source_target_pairs={{0,1},{1,0},{2,3},{3,2},{4,5},{5,4},{6,7},{7,6},{8,9},{9,8},{10,11... | collective-permute-start | bytes 1572872 | tf_op jit(solution)/shard_map/ppermute | solution.py:37
  59.2 8.0 %collective-permute-start.22 = (bf16[8,64,128]{2,1,0:T(8,128)(2,1)S(1)}, bf16[8,64,128]{2,1,0:T(8,128)(2,1)S(1)}, u32[]{:S(2)}, u32[]{:S(2)}) collective-permute-start(bf16[8,64,128]{2,1,0:T(8,128)(2,1)S(1)} %get-tuple-element.45), channel_id=1, source_target_pairs={{0,2},{1,3},{2,0},{3,1},{4,6},{5,7},{6,4},{7,5},{8,10},{9,11},{10,... | collective-permute-start | bytes 393224 | tf_op jit(solution)/shard_map/ppermute | solution.py:37
  60.7 8.1 %collective-permute-start.23 = (bf16[8,64,128]{2,1,0:T(8,128)(2,1)S(1)}, bf16[8,64,128]{2,1,0:T(8,128)(2,1)S(1)}, u32[]{:S(2)}, u32[]{:S(2)}) collective-permute-start(bf16[8,64,128]{2,1,0:T(8,128)(2,1)S(1)} %get-tuple-element.46), channel_id=1, source_target_pairs={{0,4},{1,5},{2,6},{3,7},{4,0},{5,1},{6,2},{7,3},{8,12},{9,13},{10,... | collective-permute-start | bytes 393224 | tf_op jit(solution)/shard_map/ppermute | solution.py:37
  62.2 6.6 %collective-permute-start.24 = (bf16[8,64,128]{2,1,0:T(8,128)(2,1)S(1)}, bf16[8,64,128]{2,1,0:T(8,128)(2,1)S(1)}, u32[]{:S(2)}, u32[]{:S(2)}) collective-permute-start(bf16[8,64,128]{2,1,0:T(8,128)(2,1)S(1)} %get-tuple-element.47), channel_id=1, source_target_pairs={{0,6},{1,7},{2,4},{3,5},{4,2},{5,3},{6,0},{7,1},{8,14},{9,15},{10,... | collective-permute-start | bytes 393224 | tf_op jit(solution)/shard_map/ppermute | solution.py:37
  64.1 6.3 %collective-permute-start.25 = (bf16[8,64,128]{2,1,0:T(8,128)(2,1)S(1)}, bf16[8,64,128]{2,1,0:T(8,128)(2,1)S(1)}, u32[]{:S(2)}, u32[]{:S(2)}) collective-permute-start(bf16[8,64,128]{2,1,0:T(8,128)(2,1)S(1)} %get-tuple-element.48), channel_id=1, source_target_pairs={{0,8},{8,0},{16,24},{24,16},{1,9},{9,1},{17,25},{25,17},{2,10},{10... | collective-permute-start | bytes 393224 | tf_op jit(solution)/shard_map/ppermute | solution.py:37
  66.1 12.4 %collective-permute-start.26 = (bf16[8,64,128]{2,1,0:T(8,128)(2,1)S(1)}, bf16[8,64,128]{2,1,0:T(8,128)(2,1)S(1)}, u32[]{:S(2)}, u32[]{:S(2)}) collective-permute-start(bf16[8,64,128]{2,1,0:T(8,128)(2,1)S(1)} %get-tuple-element.49), channel_id=1, source_target_pairs={{0,16},{8,24},{16,0},{24,8},{1,17},{9,25},{17,1},{25,9},{2,18},{10... | collective-permute-start | bytes 393224 | tf_op jit(solution)/shard_map/ppermute | solution.py:37
  67.1 11.4 %collective-permute-start.27 = (bf16[8,64,128]{2,1,0:T(8,128)(2,1)S(1)}, bf16[8,64,128]{2,1,0:T(8,128)(2,1)S(1)}, u32[]{:S(2)}, u32[]{:S(2)}) collective-permute-start(bf16[8,64,128]{2,1,0:T(8,128)(2,1)S(1)} %get-tuple-element.50), channel_id=1, source_target_pairs={{0,24},{8,16},{16,8},{24,0},{1,25},{9,17},{17,9},{25,1},{2,26},{10... | collective-permute-start | bytes 393224 | tf_op jit(solution)/shard_map/ppermute | solution.py:37
  79.3 5.9 %collective-permute-start.30 = (bf16[8,64,128]{2,1,0:T(8,128)(2,1)S(1)}, bf16[8,64,128]{2,1,0:T(8,128)(2,1)S(1)}, u32[]{:S(2)}, u32[]{:S(2)}) collective-permute-start(bf16[8,64,128]{2,1,0:T(8,128)(2,1)S(1)} %get-tuple-element.52.refs_2_), channel_id=1, source_target_pairs={{0,6},{1,7},{2,4},{3,5},{4,2},{5,3},{6,0},{7,1},{8,14},{9,15},{10,... | collective-permute-start | bytes 393224 | tf_op jit(solution)/shard_map/ppermute | solution.py:37
  81.8 5.0 %collective-permute-start.29 = (bf16[8,64,128]{2,1,0:T(8,128)(2,1)S(1)}, bf16[8,64,128]{2,1,0:T(8,128)(2,1)S(1)}, u32[]{:S(2)}, u32[]{:S(2)}) collective-permute-start(bf16[8,64,128]{2,1,0:T(8,128)(2,1)S(1)} %get-tuple-element.52.refs_2_), channel_id=1, source_target_pairs={{0,4},{1,5},{2,6},{3,7},{4,0},{5,1},{6,2},{7,3},{8,12},{9,13},{10,... | collective-permute-start | bytes 393224 | tf_op jit(solution)/shard_map/ppermute | solution.py:37
  82.3 5.0 %collective-permute-start.28 = (bf16[8,64,128]{2,1,0:T(8,128)(2,1)S(1)}, bf16[8,64,128]{2,1,0:T(8,128)(2,1)S(1)}, u32[]{:S(2)}, u32[]{:S(2)}) collective-permute-start(bf16[8,64,128]{2,1,0:T(8,128)(2,1)S(1)} %get-tuple-element.52.refs_2_), channel_id=1, source_target_pairs={{0,2},{1,3},{2,0},{3,1},{4,6},{5,7},{6,4},{7,5},{8,10},{9,11},{10,... | collective-permute-start | bytes 393224 | tf_op jit(solution)/shard_map/ppermute | solution.py:37
  87.3 15.1 %collective-permute-start.31 = (bf16[4,8,64,128]{3,2,1,0:T(8,128)(2,1)S(1)}, bf16[4,8,64,128]{3,2,1,0:T(8,128)(2,1)S(1)}, u32[]{:S(2)}, u32[]{:S(2)}) collective-permute-start(bf16[4,8,64,128]{3,2,1,0:T(8,128)(2,1)S(1)} %pad_maximum_fusion.2.refs_0_), channel_id=1, source_target_pairs={{0,1},{1,0},{2,3},{3,2},{4,5},{5,4},{6,7},{7,6},{8,9},{9,8},{10,11... | collective-permute-start | bytes 1572872 | tf_op jit(solution)/shard_map/ppermute | solution.py:37
  87.4 8.5 %collective-permute-start.32 = (bf16[8,64,128]{2,1,0:T(8,128)(2,1)S(1)}, bf16[8,64,128]{2,1,0:T(8,128)(2,1)S(1)}, u32[]{:S(2)}, u32[]{:S(2)}) collective-permute-start(bf16[8,64,128]{2,1,0:T(8,128)(2,1)S(1)} %get-tuple-element.52.refs_2_), channel_id=1, source_target_pairs={{0,8},{8,0},{16,24},{24,16},{1,9},{9,1},{17,25},{25,17},{2,10},{10... | collective-permute-start | bytes 393224 | tf_op jit(solution)/shard_map/ppermute | solution.py:37
  89.6 12.9 %collective-permute-start.33 = (bf16[8,64,128]{2,1,0:T(8,128)(2,1)S(1)}, bf16[8,64,128]{2,1,0:T(8,128)(2,1)S(1)}, u32[]{:S(2)}, u32[]{:S(2)}) collective-permute-start(bf16[8,64,128]{2,1,0:T(8,128)(2,1)S(1)} %get-tuple-element.52.refs_2_), channel_id=1, source_target_pairs={{0,16},{8,24},{16,0},{24,8},{1,17},{9,25},{17,1},{25,9},{2,18},{10... | collective-permute-start | bytes 393224 | tf_op jit(solution)/shard_map/ppermute | solution.py:37
  90.9 11.6 %collective-permute-start.34 = (bf16[8,64,128]{2,1,0:T(8,128)(2,1)S(1)}, bf16[8,64,128]{2,1,0:T(8,128)(2,1)S(1)}, u32[]{:S(2)}, u32[]{:S(2)}) collective-permute-start(bf16[8,64,128]{2,1,0:T(8,128)(2,1)S(1)} %get-tuple-element.52.refs_2_), channel_id=1, source_target_pairs={{0,24},{8,16},{16,8},{24,0},{1,25},{9,17},{17,9},{25,1},{2,26},{10... | collective-permute-start | bytes 393224 | tf_op jit(solution)/shard_map/ppermute | solution.py:37
  104.3 1.3 collective-permute-start.35
  105.6 4.3 %collective-permute-start.36 = (f32[64,192]{1,0:T(8,128)S(1)}, f32[64,192]{1,0:T(8,128)S(1)}, u32[]{:S(2)}, u32[]{:S(2)}) collective-permute-start(f32[64,192]{1,0:T(8,128)S(1)} %add.30), channel_id=1, source_target_pairs={{0,2},{1,3},{2,0},{3,1},{4,6},{5,7},{6,4},{7,5},{8,10},{9,11},{10,... | collective-permute-start | bytes 147464 | tf_op jit(solution)/shard_map/ppermute | solution.py:37
  109.9 4.3 %collective-permute-start.37 = (f32[64,192]{1,0:T(8,128)S(1)}, f32[64,192]{1,0:T(8,128)S(1)}, u32[]{:S(2)}, u32[]{:S(2)}) collective-permute-start(f32[64,192]{1,0:T(8,128)S(1)} %add.31), channel_id=1, source_target_pairs={{0,4},{1,5},{2,6},{3,7},{4,0},{5,1},{6,2},{7,3},{8,12},{9,13},{10,... | collective-permute-start | bytes 147464 | tf_op jit(solution)/shard_map/ppermute | solution.py:37
  114.3 4.9 %collective-permute-start.38 = (f32[64,192]{1,0:T(8,128)S(1)}, f32[64,192]{1,0:T(8,128)S(1)}, u32[]{:S(2)}, u32[]{:S(2)}) collective-permute-start(f32[64,192]{1,0:T(8,128)S(1)} %add.32), channel_id=1, source_target_pairs={{0,8},{8,0},{16,24},{24,16},{1,9},{9,1},{17,25},{25,17},{2,10},{10... | collective-permute-start | bytes 147464 | tf_op jit(solution)/shard_map/ppermute | solution.py:37
  119.2 6.0 %collective-permute-start.39 = (f32[64,192]{1,0:T(8,128)S(1)}, f32[64,192]{1,0:T(8,128)S(1)}, u32[]{:S(2)}, u32[]{:S(2)}) collective-permute-start(f32[64,192]{1,0:T(8,128)S(1)} %add.33), channel_id=1, source_target_pairs={{0,16},{8,24},{16,0},{24,8},{1,17},{9,25},{17,1},{25,9},{2,18},{10... | collective-permute-start | bytes 147464 | tf_op jit(solution)/shard_map/ppermute | solution.py:37
  138.2 1.3 copy-start.5

commit v4 on v3

--- a/solution.py
+++ b/solution.py
@@ -16,20 +16,21 @@
 F32 = jnp.float32
 VMEM = pl.BlockSpec(memory_space=pltpu.VMEM)
 SMEM = pl.BlockSpec(memory_space=pltpu.SMEM)
+ANY = pl.BlockSpec(memory_space=pl.ANY)
 DEGREE_ROWS = 16
 
 
-def call(kernel, out_shape, scratch, limit, args, flops=0, smem=0):
+def call(kernel, out_shape, scratch, limit, args, flops=0, smem=0, after=()):
     moved = sum(x.size * x.dtype.itemsize for x in args)
     return pl.pallas_call(
-        kernel,
+        lambda *refs: kernel(*refs[len(after) :]),
         out_shape=out_shape,
-        in_specs=[SMEM] * smem + [VMEM] * (len(args) - smem),
+        in_specs=[ANY] * len(after) + [SMEM] * smem + [VMEM] * (len(args) - smem),
         out_specs=jax.tree.map(lambda _: VMEM, out_shape),
         scratch_shapes=scratch,
         compiler_params=pltpu.CompilerParams(vmem_limit_bytes=limit * 2**20),
         cost_estimate=pl.CostEstimate(flops=flops, bytes_accessed=moved, transcendentals=0),
-    )(*args)
+    )(*after, *args)
 
 
 def trade(part, axis, d):
@@ -112,7 +113,7 @@
             send[group] = split_degree(degree_of(total, d * group, group, vectors_n), vectors_n)
 
 
-def products(tiles, in_rows, out_rows, meta, parts, group, out_n, dims, halves, degree):
+def products(tiles, in_rows, out_rows, meta, parts, group, out_n, dims, halves, degree, after=()):
     vectors_n, width = parts[0].shape[-2:]
     height = vectors_n + (DEGREE_ROWS if degree else 0)
     blocks = group + (1 if degree else 0)
@@ -133,7 +134,7 @@
     kernel = functools.partial(product_kernel, len(parts), degree, dims, halves)
     flops = 2 * tiles.size * height
     args = [meta, in_rows, out_rows, tiles, *parts]
-    own, *send = call(kernel, out_shape, scratch, 24, args, flops, 3)
+    own, *send = call(kernel, out_shape, scratch, 24, args, flops, 3, after)
     return own, send
 
 
@@ -216,34 +217,88 @@
     )
 
 
-def form_kernel(parts_n, halves, meta, tile_rows, tile_cols, tiles_ref, gram_ref, *refs):
-    part_refs, (out_ref, panel, left, right) = refs[:parts_n], refs[parts_n:]
-    group, (_, vectors_n, width) = part_refs[-1].shape[0], panel.shape
-    place_at = 0
-    for part in part_refs:
-        blocks = part.reshape(-1, vectors_n, width)
-        panel[place_at : place_at + blocks.shape[0]] = blocks[...]
-        place_at += blocks.shape[0]
-    cols_at = 2 * halves * group
+def half_form_kernel(halves, meta, tile_rows, tiles_ref, own_parts, other_parts, out_ref, panel):
+    _, group, vectors_n, width = own_parts.shape
+    for d in range(halves):
+        panel[d * group : (d + 1) * group] = own_parts[d]
+        panel[(halves + d) * group : (halves + d + 1) * group] = other_parts[d]
     for t in range(tiles_ref.shape[0]):
         row = place(tile_rows[t], group, meta[1], halves)
-        col = place(tile_cols[t], group, meta[0], 0) + cols_at
-        columns = slice(t * width, (t + 1) * width)
-        left[:, columns] = panel[row]
-        right[:, columns] = lax.dot_general(
-            panel[col], tiles_ref[t], NT, preferred_element_type=F32
+        out_ref[:, t * width : (t + 1) * width] = lax.dot_general(
+            panel[row], tiles_ref[t], NN, preferred_element_type=F32
         ).astype(BF16)
+
+
+def form_kernel(parts_n, meta, tile_cols, left, gram_ref, *refs):
+    part_refs, (out_ref, panel, right) = refs[:parts_n], refs[parts_n:]
+    group, vectors_n, width = part_refs[0].shape
+    for d, part in enumerate(part_refs):
+        panel[d * group : (d + 1) * group] = part[...]
+    for t in range(right.shape[1] // width):
+        right[:, t * width : (t + 1) * width] = panel[place(tile_cols[t], group, meta[0], 0)]
     form = lax.dot_general(left[...], right[...], NT, preferred_element_type=F32)
-    out_ref[...] = jnp.concatenate([gram_ref[...], form], 1)
-
-
-def all_sum(part):
-    for axis in ("col", "row"):
-        d = 1
-        while d < lax.axis_size(axis):
-            part = part + trade(part, axis, d)
-            d *= 2
-    return part
+    swapped = lax.dot_general(right[...], left[...], NT, preferred_element_type=F32)
+    projected = gram_ref[:, vectors_n:] - 0.5 * (form + swapped)
+    row, col = square_index(vectors_n)
+    packed = jnp.where(col >= row, gram_ref[:, :vectors_n], projected)
+    diagonal = jnp.sum(jnp.where(row == col, projected, 0.0), 0, keepdims=True)
+    half = vectors_n // 2
+    out_ref[:half] = jnp.concatenate([packed[:half], packed[half:]], 1)
+    diagonal = jnp.broadcast_to(diagonal, (8, vectors_n))
+    out_ref[half:] = jnp.concatenate([diagonal, jnp.zeros_like(diagonal)], 1)
+
+
+def square_index(n):
+    return tuple(lax.broadcasted_iota(jnp.int32, (n, n), axis) for axis in (0, 1))
+
+
+def inverse_factor(gram):
+    n = gram.shape[0]
+    row, col = square_index(n)
+    table = jnp.concatenate([gram, jnp.where(row == col, 1.0, 0.0)], 1)
+    bands = [table[i : i + 8] for i in range(0, n, 8)]
+    below = lax.broadcasted_iota(jnp.int32, (8, 2 * n), 0)
+    for j in range(n):
+        at, line = j // 8, j % 8
+        pivot_row = bands[at][line : line + 1, :]
+        pivot_row = jnp.broadcast_to(pivot_row / pivot_row[:, j : j + 1], (8, 2 * n))
+        for i in range(at, n // 8):
+            update = bands[i][:, j : j + 1] * pivot_row
+            if i == at:
+                update = jnp.where(below > line, update, 0.0)
+            bands[i] = bands[i] - update
+    table = jnp.concatenate(bands, 0)
+    pivots = jnp.sum(jnp.where(row == col, table[:, :n], 0.0), 1, keepdims=True)
+    return table[:, n:] / jnp.sqrt(pivots)
+
+
+def last_kernel(total_nodes, filtered_ref, *refs):
+    parts, (ritz_ref, rayleigh_ref) = refs[:-2], refs[-2:]
+    n = filtered_ref.shape[0]
+    half = n // 2
+    sums = tree_sum([part[...] for part in parts]) * (1.0 / total_nodes)
+    packed = jnp.concatenate([sums[:half, :n], sums[:half, n:]], 0)
+    row, col = square_index(n)
+    upper = jnp.where(col > row, packed, 0.0)
+    gram = jnp.where(col >= row, packed, 0.0) + upper.T
+    lower = jnp.where(col < row, packed, 0.0)
+    diagonal = jnp.broadcast_to(sums[half : half + 1, :n], (n, n))
+    projected = lower + lower.T + jnp.where(row == col, diagonal, 0.0)
+    inverse = inverse_factor(gram)
+
+    def dot(a, b, dims):
+        return lax.dot_general(a, b, dims, precision=HIGHEST, preferred_element_type=F32)
+
+    half_way = dot(inverse, projected, NN)
+    rayleigh_ref[...] = dot(half_way, inverse, NT)
+    turned = dot(inverse, half_way, NT)
+    ritz_ref[...] = dot(dot(turned, inverse, NN), filtered_ref[...], NN)
+
+
+def tree_sum(parts):
+    while len(parts) > 1:
+        parts = [a + b for a, b in zip(parts[::2], parts[1::2])]
+    return parts[0]
 
 
 def local(tiles, tile_rows, tile_cols, start):
@@ -274,7 +329,17 @@
         )
         col_got = exchange(col_send, "row")
         kept, (send,) = products(
-            tiles, tile_cols, tile_rows, meta, col_parts, group, cols_n, NT, (0, chips_n), degree
+            tiles,
+            tile_cols,
+            tile_rows,
+            meta,
+            col_parts,
+            group,
+            cols_n,
+            NT,
+            (0, chips_n),
+            degree,
+            [col_own],
         )
         row_own, row_send = merge(kept, trade(send, "col", 1), degree)
         row_got = exchange(row_send, "col", 2)
@@ -298,35 +363,34 @@
         [start, first, degree, *sums],
     )
     col_parts, row_parts = gather(rounded)
-    parts = [*row_parts, *col_parts]
     spread = (vectors_n, tiles.shape[0] * width)
-    form = call(
-        functools.partial(form_kernel, len(parts), chips_n),
-        jax.ShapeDtypeStruct((vectors_n, 3 * vectors_n), F32),
-        [
-            pltpu.VMEM(((cols_n + rows_n) * group, vectors_n, width), BF16),
-            pltpu.VMEM(spread, BF16),
-            pltpu.VMEM(spread, BF16),
-        ],
+    left = call(
+        functools.partial(half_form_kernel, chips_n),
+        jax.ShapeDtypeStruct(spread, BF16),
+        [pltpu.VMEM((cols_n * group, vectors_n, width), BF16)],
         24,
-        [meta, tile_rows, tile_cols, tiles, gram, *parts],
+        [meta, tile_rows, tiles, *row_parts],
         2 * tiles.size * vectors_n,
-        3,
-    )
-    sums = all_sum(form) / total_nodes
-    gram, scaled, form = (sums[:, i * vectors_n : (i + 1) * vectors_n] for i in range(3))
-    factor = jnp.linalg.cholesky(gram)
-    inverse = jax.scipy.linalg.solve_triangular(
-        factor, jnp.eye(vectors_n, dtype=F32), lower=True
-    )
-    projected = scaled - 0.5 * (form + form.T)
-    rayleigh = jnp.dot(
-        jnp.dot(inverse, projected, precision=HIGHEST), inverse.T, precision=HIGHEST
-    )
-    ritz = jnp.dot(
-        jnp.dot(rayleigh.T, inverse, precision=HIGHEST), filtered, precision=HIGHEST
-    )
-    return (ritz, rayleigh)
+        2,
+    )
+    sums = call(
+        functools.partial(form_kernel, rows_n),
+        jax.ShapeDtypeStruct((vectors_n // 2 + 8, 2 * vectors_n), F32),
+        [pltpu.VMEM((rows_n * group, vectors_n, width), BF16), pltpu.VMEM(spread, BF16)],
+        24,
+        [meta, tile_cols, left, gram, *col_parts],
+        4 * vectors_n * tiles.size // width,
+        2,
+    )
+    sums = sums + trade(sums, "col", 1)
+    sums = tree_sum([sums, *exchange([sums] * (chips_n - 1), "col", 2)])
+    return call(
+        functools.partial(last_kernel, total_nodes),
+        [vector_shape, jax.ShapeDtypeStruct((vectors_n, vectors_n), F32)],
+        [],
+        24,
+        [filtered, sums, *exchange([sums] * (rows_n - 1), "row")],
+    )
 
 
 def solution(mesh):

time: 140 us -> 133 us (0.950)
  other arithmetic: 12.5 us -> 0.36 us
  Pallas kernels: 9.17 us -> 16.9 us
  waiting for transfers between devices: 56.9 us -> 63.8 us
  starting transfers between devices: 56.9 us -> 50.1 us
  matrix products: 1.95 us -> 0 us
    another operation x5 -> x0, other arithmetic: 12.1 us -> none  [the longest x3 6.52 us: local(): factor = jnp.linalg.cholesky(gram)]
    pallas_call x10 -> x12, Pallas kernels: 9.17 us -> 16.9 us  [call(): pl.pallas_call(lambda *refs: kernel(*refs[len(after):]), out_shape=out_sh...]
    ppermute x40 -> x42, waiting for transfers between devices: 56.9 us -> 63.8 us  [trade(): return lax.ppermute(part, axis, [(i, i ^ d) for i in range(n)])]
    ppermute x40 -> x42, starting transfers between devices: 56.9 us -> 50.1 us  [trade(): return lax.ppermute(part, axis, [(i, i ^ d) for i in range(n)])]
    dot_general x4 -> x0, matrix products: 1.73 us -> none  [the longest x1 1.06 us: local(): jnp.dot(jnp.dot(rayleigh.T, inverse, precision=HIGHEST), filtered, precis...]
  transfers between devices with their start and end apart: 40 -> 42, of which waited for: 18 -> 26; matrix products, arithmetic and copies ran while one was open for 0% -> 0% of each run, Pallas kernels for 5% -> 3%
where the time goes in v4:
time: 133 us
  waiting for transfers between devices  63.8 us (48%)
  starting transfers between devices  50.1 us (38%)
  Pallas kernels  16.9 us (13%)
    ppermute x42, waiting for transfers between devices, trade(): return lax.ppermute(part, axis, [(i, i ^ d) for i in range(n)])  63.8 us
    ppermute x42, starting transfers between devices, trade(): return lax.ppermute(part, axis, [(i, i ^ d) for i in range(n)])  50.1 us
    pallas_call x12, Pallas kernels, call(): pl.pallas_call(lambda *refs: kernel(*refs[len(after):]), out_shape=out_sh...  16.9 us
  transfers between devices with their start and end apart: 42, of which 26 were waited for; matrix products, arithmetic and copies ran while one was open for 0% of the time, Pallas kernels for 3%

profile of v4, /device:TPU:0, one launch (start us, length us, event | category | flops | bytes accessed | tf_op | source)
XLA Modules:
  0.0 132.9 jit_solution(16187577198542155321)
XLA Ops:
  1.6 4.0 %collective-permute-start.2 = (bf16[8,64,128]{2,1,0:T(8,128)(2,1)S(1)}, bf16[8,64,128]{2,1,0:T(8,128)(2,1)S(1)}, u32[]{:S(2)}, u32[]{:S(2)}) collective-permute-start(bf16[8,64,128]{2,1,0:T(8,128)(2,1)S(1)} %shard_map.59.refs_5_), channel_id=1, source_target_pairs={{0,6},{1,7},{2,4},{3,5},{4,2},{5,3},{6,0},{7,1},{8,14},{9,15},{10,... | collective-permute-start | bytes 393224 | tf_op jit(solution)/shard_map/ppermute | solution.py:38
  6.2 3.3 %collective-permute-done.2 = bf16[8,64,128]{2,1,0:T(8,128)(2,1)S(1)} collective-permute-done((bf16[8,64,128]{2,1,0:T(8,128)(2,1)S(1)}, bf16[8,64,128]{2,1,0:T(8,128)(2,1)S(1)}, u32[]{:S(2)}, u32[]{:S(2)}) %collective-permute-start.2) | collective-permute-done | bytes 131104 | tf_op jit(solution)/shard_map/ppermute | solution.py:38
  9.5 2.4 %collective-permute-done.1 = bf16[8,64,128]{2,1,0:T(8,128)(2,1)S(1)} collective-permute-done((bf16[8,64,128]{2,1,0:T(8,128)(2,1)S(1)}, bf16[8,64,128]{2,1,0:T(8,128)(2,1)S(1)}, u32[]{:S(2)}, u32[]{:S(2)}) %collective-permute-start.1) | collective-permute-done | bytes 131104 | tf_op jit(solution)/shard_map/ppermute | solution.py:38
  12.3 3.7 %collective-permute-start.6 = (bf16[8,64,128]{2,1,0:T(8,128)(2,1)S(1)}, bf16[8,64,128]{2,1,0:T(8,128)(2,1)S(1)}, u32[]{:S(2)}, u32[]{:S(2)}) collective-permute-start(bf16[8,64,128]{2,1,0:T(8,128)(2,1)S(1)} %shard_map.59.refs_5_), channel_id=1, source_target_pairs={{0,24},{8,16},{16,8},{24,0},{1,25},{9,17},{17,9},{25,1},{2,26},{10... | collective-permute-start | bytes 393224 | tf_op jit(solution)/shard_map/ppermute | solution.py:38
  16.9 1.5 %shard_map.60 = (f32[8,80,128]{2,1,0:T(8,128)S(1)}, bf16[9,64,128]{2,1,0:T(8,128)(2,1)S(1)}, bf16[9,64,128]{2,1,0:T(8,128)(2,1)S(1)}, bf16[9,64,128]{2,1,0:T(8,128)(2,1)S(1)}) custom-call(s32[2]{0:T(128)S(1)} %pad_add_fusion.refs_0_, s32[32]{0:T(128)S(1)} %bitcast.30, s32[32]{0:T(128)S(1)} %bitcast.25, bf16[32,128,128]{2,1,0:T(8,128)(2,1)S(1)} %bitcast.17, ...), custom_call_target="tpu_custom_call" | custom-call | flops 83886080 | bytes 2097416 | tf_op jit(solution)/shard_map/pallas_call | solution.py:25
  18.4 2.1 %collective-permute-done.6.refs_8_ = bf16[8,64,128]{2,1,0:T(8,128)(2,1)S(1)} collective-permute-done((bf16[8,64,128]{2,1,0:T(8,128)(2,1)S(1)}, bf16[8,64,128]{2,1,0:T(8,128)(2,1)S(1)}, u32[]{:S(2)}, u32[]{:S(2)}) %collective-permute-start.6) | collective-permute-done | bytes 131104 | tf_op jit(solution)/shard_map/ppermute | solution.py:38
  20.5 7.1 %collective-permute-done.5.refs_7_ = bf16[8,64,128]{2,1,0:T(8,128)(2,1)S(1)} collective-permute-done((bf16[8,64,128]{2,1,0:T(8,128)(2,1)S(1)}, bf16[8,64,128]{2,1,0:T(8,128)(2,1)S(1)}, u32[]{:S(2)}, u32[]{:S(2)}) %collective-permute-start.5) | collective-permute-done | bytes 131104 | tf_op jit(solution)/shard_map/ppermute | solution.py:38
  27.6 1.8 %shard_map.61 = (f32[4,8,80,128]{3,2,1,0:T(8,128)S(1)}, bf16[4,9,64,128]{3,2,1,0:T(8,128)(2,1)S(1)}) custom-call(f32[8,80,128]{2,1,0:T(8,128)S(1)} %get-tuple-element.28.refs_0_.refs_2_, s32[2]{0:T(128)S(1)} %pad_add_fusion.1.refs_1_.refs_0_, s32[32]{0:T(128)S(1)} %bitcast.26, s32[32]{0:T(128)S(1)} %bitcast.31, bf16[32,128,128]{2,1,0:T(8,128)(2,1)S(1)} %bitcast.18, ...), custom_call_target="tpu_custom_call" | custom-call | flops 83886080 | bytes 1573128 | tf_op jit(solution)/shard_map/pallas_call | solution.py:25
  29.6 3.0 %collective-permute-start.12 = (bf16[9,64,128]{2,1,0:T(8,128)(2,1)S(1)}, bf16[9,64,128]{2,1,0:T(8,128)(2,1)S(1)}, u32[]{:S(2)}, u32[]{:S(2)}) collective-permute-start(bf16[9,64,128]{2,1,0:T(8,128)(2,1)S(1)} %get-tuple-element.36), channel_id=1, source_target_pairs={{0,16},{8,24},{16,0},{24,8},{1,17},{9,25},{17,1},{25,9},{2,18},{10... | collective-permute-start | bytes 442376 | tf_op jit(solution)/shard_map/ppermute | solution.py:38
  32.6 1.3 %collective-permute-start.13 = (bf16[9,64,128]{2,1,0:T(8,128)(2,1)S(1)}, bf16[9,64,128]{2,1,0:T(8,128)(2,1)S(1)}, u32[]{:S(2)}, u32[]{:S(2)}) collective-permute-start(bf16[9,64,128]{2,1,0:T(8,128)(2,1)S(1)} %get-tuple-element.37), channel_id=1, source_target_pairs={{0,24},{8,16},{16,8},{24,0},{1,25},{9,17},{17,9},{25,1},{2,26},{10... | collective-permute-start | bytes 442376 | tf_op jit(solution)/shard_map/ppermute | solution.py:38
  34.1 1.6 %collective-permute-start.8 = (bf16[9,64,128]{2,1,0:T(8,128)(2,1)S(1)}, bf16[9,64,128]{2,1,0:T(8,128)(2,1)S(1)}, u32[]{:S(2)}, u32[]{:S(2)}) collective-permute-start(bf16[9,64,128]{2,1,0:T(8,128)(2,1)S(1)} %get-tuple-element.32), channel_id=1, source_target_pairs={{0,2},{1,3},{2,0},{3,1},{4,6},{5,7},{6,4},{7,5},{8,10},{9,11},{10,... | collective-permute-start | bytes 442376 | tf_op jit(solution)/shard_map/ppermute | solution.py:38
  36.4 2.2 %collective-permute-done.11.refs_6_ = bf16[9,64,128]{2,1,0:T(8,128)(2,1)S(1)} collective-permute-done((bf16[9,64,128]{2,1,0:T(8,128)(2,1)S(1)}, bf16[9,64,128]{2,1,0:T(8,128)(2,1)S(1)}, u32[]{:S(2)}, u32[]{:S(2)}) %collective-permute-start.11) | collective-permute-done | bytes 147488 | tf_op jit(solution)/shard_map/ppermute | solution.py:38
  38.6 1.7 %collective-permute-start.10 = (bf16[9,64,128]{2,1,0:T(8,128)(2,1)S(1)}, bf16[9,64,128]{2,1,0:T(8,128)(2,1)S(1)}, u32[]{:S(2)}, u32[]{:S(2)}) collective-permute-start(bf16[9,64,128]{2,1,0:T(8,128)(2,1)S(1)} %get-tuple-element.34), channel_id=1, source_target_pairs={{0,6},{1,7},{2,4},{3,5},{4,2},{5,3},{6,0},{7,1},{8,14},{9,15},{10,... | collective-permute-start | bytes 442376 | tf_op jit(solution)/shard_map/ppermute | solution.py:38
  40.3 3.3 %collective-permute-done.12.refs_7_ = bf16[9,64,128]{2,1,0:T(8,128)(2,1)S(1)} collective-permute-done((bf16[9,64,128]{2,1,0:T(8,128)(2,1)S(1)}, bf16[9,64,128]{2,1,0:T(8,128)(2,1)S(1)}, u32[]{:S(2)}, u32[]{:S(2)}) %collective-permute-start.12) | collective-permute-done | bytes 147488 | tf_op jit(solution)/shard_map/ppermute | solution.py:38
  43.6 1.3 collective-permute-done.10.refs_5_
  45.1 1.8 %collective-permute-start.16 = (bf16[8,64,128]{2,1,0:T(8,128)(2,1)S(1)}, bf16[8,64,128]{2,1,0:T(8,128)(2,1)S(1)}, u32[]{:S(2)}, u32[]{:S(2)}) collective-permute-start(bf16[8,64,128]{2,1,0:T(8,128)(2,1)S(1)} %get-tuple-element.40.refs_5_), channel_id=1, source_target_pairs={{0,6},{1,7},{2,4},{3,5},{4,2},{5,3},{6,0},{7,1},{8,14},{9,15},{10,... | collective-permute-start | bytes 393224 | tf_op jit(solution)/shard_map/ppermute | solution.py:38
  46.9 1.3 collective-permute-start.15
  48.7 3.3 %collective-permute-done.16 = bf16[8,64,128]{2,1,0:T(8,128)(2,1)S(1)} collective-permute-done((bf16[8,64,128]{2,1,0:T(8,128)(2,1)S(1)}, bf16[8,64,128]{2,1,0:T(8,128)(2,1)S(1)}, u32[]{:S(2)}, u32[]{:S(2)}) %collective-permute-start.16) | collective-permute-done | bytes 131104 | tf_op jit(solution)/shard_map/ppermute | solution.py:38
  53.3 1.6 %collective-permute-start.20 = (bf16[8,64,128]{2,1,0:T(8,128)(2,1)S(1)}, bf16[8,64,128]{2,1,0:T(8,128)(2,1)S(1)}, u32[]{:S(2)}, u32[]{:S(2)}) collective-permute-start(bf16[8,64,128]{2,1,0:T(8,128)(2,1)S(1)} %get-tuple-element.40.refs_5_), channel_id=1, source_target_pairs={{0,24},{8,16},{16,8},{24,0},{1,25},{9,17},{17,9},{25,1},{2,26},{10... | collective-permute-start | bytes 393224 | tf_op jit(solution)/shard_map/ppermute | solution.py:38
  55.0 2.7 %collective-permute-start.19 = (bf16[8,64,128]{2,1,0:T(8,128)(2,1)S(1)}, bf16[8,64,128]{2,1,0:T(8,128)(2,1)S(1)}, u32[]{:S(2)}, u32[]{:S(2)}) collective-permute-start(bf16[8,64,128]{2,1,0:T(8,128)(2,1)S(1)} %get-tuple-element.40.refs_5_), channel_id=1, source_target_pairs={{0,16},{8,24},{16,0},{24,8},{1,17},{9,25},{17,1},{25,9},{2,18},{10... | collective-permute-start | bytes 393224 | tf_op jit(solution)/shard_map/ppermute | solution.py:38
  57.8 1.4 %shard_map.64 = (f32[8,64,128]{2,1,0:T(8,128)S(1)}, bf16[8,64,128]{2,1,0:T(8,128)(2,1)S(1)}, bf16[8,64,128]{2,1,0:T(8,128)(2,1)S(1)}, bf16[8,64,128]{2,1,0:T(8,128)(2,1)S(1)}) custom-call(s32[2]{0:T(128)S(1)} %pad_add_fusion.refs_0_, s32[32]{0:T(128)S(1)} %bitcast.32, s32[32]{0:T(128)S(1)} %bitcast.27, bf16[32,128,128]{2,1,0:T(8,128)(2,1)S(1)} %bitcast.19, ...), custom_call_target="tpu_custom_call" | custom-call | flops 67108864 | bytes 2097416 | tf_op jit(solution)/shard_map/pallas_call | solution.py:25
  59.2 2.4 %collective-permute-done.20.refs_8_ = bf16[8,64,128]{2,1,0:T(8,128)(2,1)S(1)} collective-permute-done((bf16[8,64,128]{2,1,0:T(8,128)(2,1)S(1)}, bf16[8,64,128]{2,1,0:T(8,128)(2,1)S(1)}, u32[]{:S(2)}, u32[]{:S(2)}) %collective-permute-start.20) | collective-permute-done | bytes 131104 | tf_op jit(solution)/shard_map/ppermute | solution.py:38
  61.6 7.9 %collective-permute-done.19.refs_7_ = bf16[8,64,128]{2,1,0:T(8,128)(2,1)S(1)} collective-permute-done((bf16[8,64,128]{2,1,0:T(8,128)(2,1)S(1)}, bf16[8,64,128]{2,1,0:T(8,128)(2,1)S(1)}, u32[]{:S(2)}, u32[]{:S(2)}) %collective-permute-start.19) | collective-permute-done | bytes 131104 | tf_op jit(solution)/shard_map/ppermute | solution.py:38
  69.5 1.5 %shard_map.65 = (f32[4,8,64,128]{3,2,1,0:T(8,128)S(1)}, bf16[4,8,64,128]{3,2,1,0:T(8,128)(2,1)S(1)}) custom-call(f32[8,64,128]{2,1,0:T(8,128)S(1)} %get-tuple-element.41.refs_0_.refs_4_, s32[2]{0:T(128)S(1)} %pad_add_fusion.1.refs_1_.refs_0_, s32[32]{0:T(128)S(1)} %bitcast.28, s32[32]{0:T(128)S(1)} %bitcast.33, bf16[32,128,128]{2,1,0:T(8,128)(2,1)S(1)} %bitcast.20, ...), custom_call_target="tpu_custom_call" | custom-call | flops 67108864 | bytes 1573128 | tf_op jit(solution)/shard_map/pallas_call | solution.py:25
  71.1 2.1 %collective-permute-start.26 = (bf16[8,64,128]{2,1,0:T(8,128)(2,1)S(1)}, bf16[8,64,128]{2,1,0:T(8,128)(2,1)S(1)}, u32[]{:S(2)}, u32[]{:S(2)}) collective-permute-start(bf16[8,64,128]{2,1,0:T(8,128)(2,1)S(1)} %get-tuple-element.49), channel_id=1, source_target_pairs={{0,16},{8,24},{16,0},{24,8},{1,17},{9,25},{17,1},{25,9},{2,18},{10... | collective-permute-start | bytes 393224 | tf_op jit(solution)/shard_map/ppermute | solution.py:38
  73.3 2.2 %collective-permute-start.27 = (bf16[8,64,128]{2,1,0:T(8,128)(2,1)S(1)}, bf16[8,64,128]{2,1,0:T(8,128)(2,1)S(1)}, u32[]{:S(2)}, u32[]{:S(2)}) collective-permute-start(bf16[8,64,128]{2,1,0:T(8,128)(2,1)S(1)} %get-tuple-element.50), channel_id=1, source_target_pairs={{0,24},{8,16},{16,8},{24,0},{1,25},{9,17},{17,9},{25,1},{2,26},{10... | collective-permute-start | bytes 393224 | tf_op jit(solution)/shard_map/ppermute | solution.py:38
  75.6 1.5 %collective-permute-start.22 = (bf16[8,64,128]{2,1,0:T(8,128)(2,1)S(1)}, bf16[8,64,128]{2,1,0:T(8,128)(2,1)S(1)}, u32[]{:S(2)}, u32[]{:S(2)}) collective-permute-start(bf16[8,64,128]{2,1,0:T(8,128)(2,1)S(1)} %get-tuple-element.45), channel_id=1, source_target_pairs={{0,2},{1,3},{2,0},{3,1},{4,6},{5,7},{6,4},{7,5},{8,10},{9,11},{10,... | collective-permute-start | bytes 393224 | tf_op jit(solution)/shard_map/ppermute | solution.py:38
  78.8 1.6 %collective-permute-start.24 = (bf16[8,64,128]{2,1,0:T(8,128)(2,1)S(1)}, bf16[8,64,128]{2,1,0:T(8,128)(2,1)S(1)}, u32[]{:S(2)}, u32[]{:S(2)}) collective-permute-start(bf16[8,64,128]{2,1,0:T(8,128)(2,1)S(1)} %get-tuple-element.47), channel_id=1, source_target_pairs={{0,6},{1,7},{2,4},{3,5},{4,2},{5,3},{6,0},{7,1},{8,14},{9,15},{10,... | collective-permute-start | bytes 393224 | tf_op jit(solution)/shard_map/ppermute | solution.py:38
  80.3 3.7 %collective-permute-done.26.refs_9_ = bf16[8,64,128]{2,1,0:T(8,128)(2,1)S(1)} collective-permute-done((bf16[8,64,128]{2,1,0:T(8,128)(2,1)S(1)}, bf16[8,64,128]{2,1,0:T(8,128)(2,1)S(1)}, u32[]{:S(2)}, u32[]{:S(2)}) %collective-permute-start.26) | collective-permute-done | bytes 131104 | tf_op jit(solution)/shard_map/ppermute | solution.py:38
  85.7 1.5 %collective-permute-start.30 = (bf16[8,64,128]{2,1,0:T(8,128)(2,1)S(1)}, bf16[8,64,128]{2,1,0:T(8,128)(2,1)S(1)}, u32[]{:S(2)}, u32[]{:S(2)}) collective-permute-start(bf16[8,64,128]{2,1,0:T(8,128)(2,1)S(1)} %get-tuple-element.52.refs_4_), channel_id=1, source_target_pairs={{0,6},{1,7},{2,4},{3,5},{4,2},{5,3},{6,0},{7,1},{8,14},{9,15},{10,... | collective-permute-start | bytes 393224 | tf_op jit(solution)/shard_map/ppermute | solution.py:38
  87.1 1.3 collective-permute-start.29
  89.2 3.1 %collective-permute-done.30 = bf16[8,64,128]{2,1,0:T(8,128)(2,1)S(1)} collective-permute-done((bf16[8,64,128]{2,1,0:T(8,128)(2,1)S(1)}, bf16[8,64,128]{2,1,0:T(8,128)(2,1)S(1)}, u32[]{:S(2)}, u32[]{:S(2)}) %collective-permute-start.30) | collective-permute-done | bytes 131104 | tf_op jit(solution)/shard_map/ppermute | solution.py:38
  92.3 1.3 collective-permute-done.29
  93.7 2.1 %collective-permute-start.34 = (bf16[8,64,128]{2,1,0:T(8,128)(2,1)S(1)}, bf16[8,64,128]{2,1,0:T(8,128)(2,1)S(1)}, u32[]{:S(2)}, u32[]{:S(2)}) collective-permute-start(bf16[8,64,128]{2,1,0:T(8,128)(2,1)S(1)} %get-tuple-element.52.refs_4_), channel_id=1, source_target_pairs={{0,24},{8,16},{16,8},{24,0},{1,25},{9,17},{17,9},{25,1},{2,26},{10... | collective-permute-start | bytes 393224 | tf_op jit(solution)/shard_map/ppermute | solution.py:38
  95.8 2.3 %collective-permute-start.33 = (bf16[8,64,128]{2,1,0:T(8,128)(2,1)S(1)}, bf16[8,64,128]{2,1,0:T(8,128)(2,1)S(1)}, u32[]{:S(2)}, u32[]{:S(2)}) collective-permute-start(bf16[8,64,128]{2,1,0:T(8,128)(2,1)S(1)} %get-tuple-element.52.refs_4_), channel_id=1, source_target_pairs={{0,16},{8,24},{16,0},{24,8},{1,17},{9,25},{17,1},{25,9},{2,18},{10... | collective-permute-start | bytes 393224 | tf_op jit(solution)/shard_map/ppermute | solution.py:38
  98.2 1.1 shard_map.68.refs_2_
  99.3 2.7 %collective-permute-done.34.refs_7_ = bf16[8,64,128]{2,1,0:T(8,128)(2,1)S(1)} collective-permute-done((bf16[8,64,128]{2,1,0:T(8,128)(2,1)S(1)}, bf16[8,64,128]{2,1,0:T(8,128)(2,1)S(1)}, u32[]{:S(2)}, u32[]{:S(2)}) %collective-permute-start.34) | collective-permute-done | bytes 131104 | tf_op jit(solution)/shard_map/ppermute | solution.py:38
  102.0 7.9 %collective-permute-done.33.refs_6_ = bf16[8,64,128]{2,1,0:T(8,128)(2,1)S(1)} collective-permute-done((bf16[8,64,128]{2,1,0:T(8,128)(2,1)S(1)}, bf16[8,64,128]{2,1,0:T(8,128)(2,1)S(1)}, u32[]{:S(2)}, u32[]{:S(2)}) %collective-permute-start.33) | collective-permute-done | bytes 131104 | tf_op jit(solution)/shard_map/ppermute | solution.py:38
  109.8 1.2 shard_map.69
  111.2 1.1 collective-permute-done.35
  112.3 1.5 %collective-permute-start.38 = (f32[40,128]{1,0:T(8,128)S(1)}, f32[40,128]{1,0:T(8,128)S(1)}, u32[]{:S(2)}, u32[]{:S(2)}) collective-permute-start(f32[40,128]{1,0:T(8,128)S(1)} %add.12), channel_id=1, source_target_pairs={{0,6},{1,7},{2,4},{3,5},{4,2},{5,3},{6,0},{7,1},{8,14},{9,15},{10,... | collective-permute-start | bytes 61448 | tf_op jit(solution)/shard_map/ppermute | solution.py:38
  113.8 1.3 collective-permute-start.37
  115.8 1.2 collective-permute-done.38
  117.6 1.3 collective-permute-done.36
  118.9 2.2 %collective-permute-start.41 = (f32[40,128]{1,0:T(8,128)S(1)}, f32[40,128]{1,0:T(8,128)S(1)}, u32[]{:S(2)}, u32[]{:S(2)}) collective-permute-start(f32[40,128]{1,0:T(8,128)S(1)} %add_add_fusion.refs_1_), channel_id=1, source_target_pairs={{0,24},{8,16},{16,8},{24,0},{1,25},{9,17},{17,9},{25,1},{2,26},{10... | collective-permute-start | bytes 61448 | tf_op jit(solution)/shard_map/ppermute | solution.py:38
  121.1 2.2 %collective-permute-start.39 = (f32[40,128]{1,0:T(8,128)S(1)}, f32[40,128]{1,0:T(8,128)S(1)}, u32[]{:S(2)}, u32[]{:S(2)}) collective-permute-start(f32[40,128]{1,0:T(8,128)S(1)} %add_add_fusion.refs_1_), channel_id=1, source_target_pairs={{0,8},{8,0},{16,24},{24,16},{1,9},{9,1},{17,25},{25,17},{2,10},{10... | collective-permute-start | bytes 61448 | tf_op jit(solution)/shard_map/ppermute | solution.py:38
  123.3 1.3 %collective-permute-done.41.refs_4_ = f32[40,128]{1,0:T(8,128)S(1)} collective-permute-done((f32[40,128]{1,0:T(8,128)S(1)}, f32[40,128]{1,0:T(8,128)S(1)}, u32[]{:S(2)}, u32[]{:S(2)}) %collective-permute-start.41) | collective-permute-done | bytes 20512 | tf_op jit(solution)/shard_map/ppermute | solution.py:38
  125.7 7.2 %shard_map.70 = (f32[64,1024]{1,0:T(8,128)}, f32[64,64]{1,0:T(8,128)}) custom-call(f32[64,1024]{1,0:T(8,128)S(1)} %get-tuple-element.51.refs_0_, f32[40,128]{1,0:T(8,128)S(1)} %add_add_fusion.refs_1_, f32[40,128]{1,0:T(8,128)S(1)} %collective-permute-done.39.refs_2_, f32[40,128]{1,0:T(8,128)S(1)} %collective-permute-done.40.refs_3_, ...), custom_call_target="tpu_custom_call" | custom-call | bytes 344064 | tf_op jit(solution)/shard_map/pallas_call | solution.py:25
  (65 shorter events, 13.1 us)
Async XLA Ops:
  0.6 1.0 copy-start.1
  1.6 15.3 %copy-start = (bf16[1,1,32,128,128]{4,3,2,1,0:T(8,128)(2,1)S(1)}, bf16[1,1,32,128,128]{4,3,2,1,0:T(8,128)(2,1)}, u32[]{:S(2)}) copy-start(bf16[1,1,32,128,128]{4,3,2,1,0:T(8,128)(2,1)} %param.4) | copy-start | bytes 3145732
  1.6 15.3 %copy-start.3 = (s32[1,1,32]{2,1,0:T(1,128)S(1)}, s32[1,1,32]{2,1,0:T(1,128)}, u32[]{:S(2)}) copy-start(s32[1,1,32]{2,1,0:T(1,128)} %param.6) | copy-start | bytes 388
  1.6 15.3 %copy-start.4 = (s32[1,1,32]{2,1,0:T(1,128)S(1)}, s32[1,1,32]{2,1,0:T(1,128)}, u32[]{:S(2)}) copy-start(s32[1,1,32]{2,1,0:T(1,128)} %param.5) | copy-start | bytes 388
  1.6 7.9 %collective-permute-start.2 = (bf16[8,64,128]{2,1,0:T(8,128)(2,1)S(1)}, bf16[8,64,128]{2,1,0:T(8,128)(2,1)S(1)}, u32[]{:S(2)}, u32[]{:S(2)}) collective-permute-start(bf16[8,64,128]{2,1,0:T(8,128)(2,1)S(1)} %shard_map.59.refs_5_), channel_id=1, source_target_pairs={{0,6},{1,7},{2,4},{3,5},{4,2},{5,3},{6,0},{7,1},{8,14},{9,15},{10,... | collective-permute-start | bytes 393224 | tf_op jit(solution)/shard_map/ppermute | solution.py:38
  5.6 6.3 %collective-permute-start.1 = (bf16[8,64,128]{2,1,0:T(8,128)(2,1)S(1)}, bf16[8,64,128]{2,1,0:T(8,128)(2,1)S(1)}, u32[]{:S(2)}, u32[]{:S(2)}) collective-permute-start(bf16[8,64,128]{2,1,0:T(8,128)(2,1)S(1)} %shard_map.59.refs_5_), channel_id=1, source_target_pairs={{0,4},{1,5},{2,6},{3,7},{4,0},{5,1},{6,2},{7,3},{8,12},{9,13},{10,... | collective-permute-start | bytes 393224 | tf_op jit(solution)/shard_map/ppermute | solution.py:38
  6.1 6.0 %collective-permute-start = (bf16[8,64,128]{2,1,0:T(8,128)(2,1)S(1)}, bf16[8,64,128]{2,1,0:T(8,128)(2,1)S(1)}, u32[]{:S(2)}, u32[]{:S(2)}) collective-permute-start(bf16[8,64,128]{2,1,0:T(8,128)(2,1)S(1)} %shard_map.59.refs_5_), channel_id=1, source_target_pairs={{0,2},{1,3},{2,0},{3,1},{4,6},{5,7},{6,4},{7,5},{8,10},{9,11},{10,... | collective-permute-start | bytes 393224 | tf_op jit(solution)/shard_map/ppermute | solution.py:38
  12.2 4.7 %collective-permute-start.3 = (bf16[4,8,64,128]{3,2,1,0:T(8,128)(2,1)S(1)}, bf16[4,8,64,128]{3,2,1,0:T(8,128)(2,1)S(1)}, u32[]{:S(2)}, u32[]{:S(2)}) collective-permute-start(bf16[4,8,64,128]{3,2,1,0:T(8,128)(2,1)S(1)} %pad_maximum_fusion.refs_4_), channel_id=1, source_target_pairs={{0,1},{1,0},{2,3},{3,2},{4,5},{5,4},{6,7},{7,6},{8,9},{9,8},{10,11... | collective-permute-start | bytes 1572872 | tf_op jit(solution)/shard_map/ppermute | solution.py:38
  12.3 8.3 %collective-permute-start.6 = (bf16[8,64,128]{2,1,0:T(8,128)(2,1)S(1)}, bf16[8,64,128]{2,1,0:T(8,128)(2,1)S(1)}, u32[]{:S(2)}, u32[]{:S(2)}) collective-permute-start(bf16[8,64,128]{2,1,0:T(8,128)(2,1)S(1)} %shard_map.59.refs_5_), channel_id=1, source_target_pairs={{0,24},{8,16},{16,8},{24,0},{1,25},{9,17},{17,9},{25,1},{2,26},{10... | collective-permute-start | bytes 393224 | tf_op jit(solution)/shard_map/ppermute | solution.py:38
  15.9 11.7 %collective-permute-start.5 = (bf16[8,64,128]{2,1,0:T(8,128)(2,1)S(1)}, bf16[8,64,128]{2,1,0:T(8,128)(2,1)S(1)}, u32[]{:S(2)}, u32[]{:S(2)}) collective-permute-start(bf16[8,64,128]{2,1,0:T(8,128)(2,1)S(1)} %shard_map.59.refs_5_), channel_id=1, source_target_pairs={{0,16},{8,24},{16,0},{24,8},{1,17},{9,25},{17,1},{25,9},{2,18},{10... | collective-permute-start | bytes 393224 | tf_op jit(solution)/shard_map/ppermute | solution.py:38
  15.9 11.7 %collective-permute-start.4 = (bf16[8,64,128]{2,1,0:T(8,128)(2,1)S(1)}, bf16[8,64,128]{2,1,0:T(8,128)(2,1)S(1)}, u32[]{:S(2)}, u32[]{:S(2)}) collective-permute-start(bf16[8,64,128]{2,1,0:T(8,128)(2,1)S(1)} %shard_map.59.refs_5_), channel_id=1, source_target_pairs={{0,8},{8,0},{16,24},{24,16},{1,9},{9,1},{17,25},{25,17},{2,10},{10... | collective-permute-start | bytes 393224 | tf_op jit(solution)/shard_map/ppermute | solution.py:38
  29.4 15.5 %copy-start.2 = (f32[64,1024]{1,0:T(8,128)S(1)}, f32[64,1024]{1,0:T(8,128)}, u32[]{:S(2)}) copy-start(f32[64,1024]{1,0:T(8,128)} %refs_0_.5) | copy-start | bytes 786436
  29.4 4.5 %collective-permute-start.7 = (bf16[4,9,64,128]{3,2,1,0:T(8,128)(2,1)S(1)}, bf16[4,9,64,128]{3,2,1,0:T(8,128)(2,1)S(1)}, u32[]{:S(2)}, u32[]{:S(2)}) collective-permute-start(bf16[4,9,64,128]{3,2,1,0:T(8,128)(2,1)S(1)} %get-tuple-element.30), channel_id=1, source_target_pairs={{0,1},{1,0},{2,3},{3,2},{4,5},{5,4},{6,7},{7,6},{8,9},{9,8},{10,11... | collective-permute-start | bytes 1769480 | tf_op jit(solution)/shard_map/ppermute | solution.py:38
  29.5 9.1 %collective-permute-start.11 = (bf16[9,64,128]{2,1,0:T(8,128)(2,1)S(1)}, bf16[9,64,128]{2,1,0:T(8,128)(2,1)S(1)}, u32[]{:S(2)}, u32[]{:S(2)}) collective-permute-start(bf16[9,64,128]{2,1,0:T(8,128)(2,1)S(1)} %get-tuple-element.35), channel_id=1, source_target_pairs={{0,8},{8,0},{16,24},{24,16},{1,9},{9,1},{17,25},{25,17},{2,10},{10... | collective-permute-start | bytes 442376 | tf_op jit(solution)/shard_map/ppermute | solution.py:38
  29.6 14.0 %collective-permute-start.12 = (bf16[9,64,128]{2,1,0:T(8,128)(2,1)S(1)}, bf16[9,64,128]{2,1,0:T(8,128)(2,1)S(1)}, u32[]{:S(2)}, u32[]{:S(2)}) collective-permute-start(bf16[9,64,128]{2,1,0:T(8,128)(2,1)S(1)} %get-tuple-element.36), channel_id=1, source_target_pairs={{0,16},{8,24},{16,0},{24,8},{1,17},{9,25},{17,1},{25,9},{2,18},{10... | collective-permute-start | bytes 442376 | tf_op jit(solution)/shard_map/ppermute | solution.py:38
  32.6 11.0 %collective-permute-start.13 = (bf16[9,64,128]{2,1,0:T(8,128)(2,1)S(1)}, bf16[9,64,128]{2,1,0:T(8,128)(2,1)S(1)}, u32[]{:S(2)}, u32[]{:S(2)}) collective-permute-start(bf16[9,64,128]{2,1,0:T(8,128)(2,1)S(1)} %get-tuple-element.37), channel_id=1, source_target_pairs={{0,24},{8,16},{16,8},{24,0},{1,25},{9,17},{17,9},{25,1},{2,26},{10... | collective-permute-start | bytes 442376 | tf_op jit(solution)/shard_map/ppermute | solution.py:38
  34.1 9.5 %collective-permute-start.8 = (bf16[9,64,128]{2,1,0:T(8,128)(2,1)S(1)}, bf16[9,64,128]{2,1,0:T(8,128)(2,1)S(1)}, u32[]{:S(2)}, u32[]{:S(2)}) collective-permute-start(bf16[9,64,128]{2,1,0:T(8,128)(2,1)S(1)} %get-tuple-element.32), channel_id=1, source_target_pairs={{0,2},{1,3},{2,0},{3,1},{4,6},{5,7},{6,4},{7,5},{8,10},{9,11},{10,... | collective-permute-start | bytes 442376 | tf_op jit(solution)/shard_map/ppermute | solution.py:38
  35.7 7.9 %collective-permute-start.9 = (bf16[9,64,128]{2,1,0:T(8,128)(2,1)S(1)}, bf16[9,64,128]{2,1,0:T(8,128)(2,1)S(1)}, u32[]{:S(2)}, u32[]{:S(2)}) collective-permute-start(bf16[9,64,128]{2,1,0:T(8,128)(2,1)S(1)} %get-tuple-element.33), channel_id=1, source_target_pairs={{0,4},{1,5},{2,6},{3,7},{4,0},{5,1},{6,2},{7,3},{8,12},{9,13},{10,... | collective-permute-start | bytes 442376 | tf_op jit(solution)/shard_map/ppermute | solution.py:38
  38.6 6.3 %collective-permute-start.10 = (bf16[9,64,128]{2,1,0:T(8,128)(2,1)S(1)}, bf16[9,64,128]{2,1,0:T(8,128)(2,1)S(1)}, u32[]{:S(2)}, u32[]{:S(2)}) collective-permute-start(bf16[9,64,128]{2,1,0:T(8,128)(2,1)S(1)} %get-tuple-element.34), channel_id=1, source_target_pairs={{0,6},{1,7},{2,4},{3,5},{4,2},{5,3},{6,0},{7,1},{8,14},{9,15},{10,... | collective-permute-start | bytes 442376 | tf_op jit(solution)/shard_map/ppermute | solution.py:38
  45.1 6.9 %collective-permute-start.16 = (bf16[8,64,128]{2,1,0:T(8,128)(2,1)S(1)}, bf16[8,64,128]{2,1,0:T(8,128)(2,1)S(1)}, u32[]{:S(2)}, u32[]{:S(2)}) collective-permute-start(bf16[8,64,128]{2,1,0:T(8,128)(2,1)S(1)} %get-tuple-element.40.refs_5_), channel_id=1, source_target_pairs={{0,6},{1,7},{2,4},{3,5},{4,2},{5,3},{6,0},{7,1},{8,14},{9,15},{10,... | collective-permute-start | bytes 393224 | tf_op jit(solution)/shard_map/ppermute | solution.py:38
  46.9 6.2 %collective-permute-start.15 = (bf16[8,64,128]{2,1,0:T(8,128)(2,1)S(1)}, bf16[8,64,128]{2,1,0:T(8,128)(2,1)S(1)}, u32[]{:S(2)}, u32[]{:S(2)}) collective-permute-start(bf16[8,64,128]{2,1,0:T(8,128)(2,1)S(1)} %get-tuple-element.40.refs_5_), channel_id=1, source_target_pairs={{0,4},{1,5},{2,6},{3,7},{4,0},{5,1},{6,2},{7,3},{8,12},{9,13},{10,... | collective-permute-start | bytes 393224 | tf_op jit(solution)/shard_map/ppermute | solution.py:38
  48.2 5.0 %collective-permute-start.14 = (bf16[8,64,128]{2,1,0:T(8,128)(2,1)S(1)}, bf16[8,64,128]{2,1,0:T(8,128)(2,1)S(1)}, u32[]{:S(2)}, u32[]{:S(2)}) collective-permute-start(bf16[8,64,128]{2,1,0:T(8,128)(2,1)S(1)} %get-tuple-element.40.refs_5_), channel_id=1, source_target_pairs={{0,2},{1,3},{2,0},{3,1},{4,6},{5,7},{6,4},{7,5},{8,10},{9,11},{10,... | collective-permute-start | bytes 393224 | tf_op jit(solution)/shard_map/ppermute | solution.py:38
  53.3 4.5 %collective-permute-start.17 = (bf16[4,8,64,128]{3,2,1,0:T(8,128)(2,1)S(1)}, bf16[4,8,64,128]{3,2,1,0:T(8,128)(2,1)S(1)}, u32[]{:S(2)}, u32[]{:S(2)}) collective-permute-start(bf16[4,8,64,128]{3,2,1,0:T(8,128)(2,1)S(1)} %pad_maximum_fusion.1.refs_4_), channel_id=1, source_target_pairs={{0,1},{1,0},{2,3},{3,2},{4,5},{5,4},{6,7},{7,6},{8,9},{9,8},{10,11... | collective-permute-start | bytes 1572872 | tf_op jit(solution)/shard_map/ppermute | solution.py:38
  53.3 8.3 %collective-permute-start.20 = (bf16[8,64,128]{2,1,0:T(8,128)(2,1)S(1)}, bf16[8,64,128]{2,1,0:T(8,128)(2,1)S(1)}, u32[]{:S(2)}, u32[]{:S(2)}) collective-permute-start(bf16[8,64,128]{2,1,0:T(8,128)(2,1)S(1)} %get-tuple-element.40.refs_5_), channel_id=1, source_target_pairs={{0,24},{8,16},{16,8},{24,0},{1,25},{9,17},{17,9},{25,1},{2,26},{10... | collective-permute-start | bytes 393224 | tf_op jit(solution)/shard_map/ppermute | solution.py:38
  55.0 14.5 %collective-permute-start.19 = (bf16[8,64,128]{2,1,0:T(8,128)(2,1)S(1)}, bf16[8,64,128]{2,1,0:T(8,128)(2,1)S(1)}, u32[]{:S(2)}, u32[]{:S(2)}) collective-permute-start(bf16[8,64,128]{2,1,0:T(8,128)(2,1)S(1)} %get-tuple-element.40.refs_5_), channel_id=1, source_target_pairs={{0,16},{8,24},{16,0},{24,8},{1,17},{9,25},{17,1},{25,9},{2,18},{10... | collective-permute-start | bytes 393224 | tf_op jit(solution)/shard_map/ppermute | solution.py:38
  57.6 11.8 %collective-permute-start.18 = (bf16[8,64,128]{2,1,0:T(8,128)(2,1)S(1)}, bf16[8,64,128]{2,1,0:T(8,128)(2,1)S(1)}, u32[]{:S(2)}, u32[]{:S(2)}) collective-permute-start(bf16[8,64,128]{2,1,0:T(8,128)(2,1)S(1)} %get-tuple-element.40.refs_5_), channel_id=1, source_target_pairs={{0,8},{8,0},{16,24},{24,16},{1,9},{9,1},{17,25},{25,17},{2,10},{10... | collective-permute-start | bytes 393224 | tf_op jit(solution)/shard_map/ppermute | solution.py:38
  71.0 4.5 %collective-permute-start.21 = (bf16[4,8,64,128]{3,2,1,0:T(8,128)(2,1)S(1)}, bf16[4,8,64,128]{3,2,1,0:T(8,128)(2,1)S(1)}, u32[]{:S(2)}, u32[]{:S(2)}) collective-permute-start(bf16[4,8,64,128]{3,2,1,0:T(8,128)(2,1)S(1)} %get-tuple-element.43), channel_id=1, source_target_pairs={{0,1},{1,0},{2,3},{3,2},{4,5},{5,4},{6,7},{7,6},{8,9},{9,8},{10,11... | collective-permute-start | bytes 1572872 | tf_op jit(solution)/shard_map/ppermute | solution.py:38
  71.1 7.7 %collective-permute-start.25 = (bf16[8,64,128]{2,1,0:T(8,128)(2,1)S(1)}, bf16[8,64,128]{2,1,0:T(8,128)(2,1)S(1)}, u32[]{:S(2)}, u32[]{:S(2)}) collective-permute-start(bf16[8,64,128]{2,1,0:T(8,128)(2,1)S(1)} %get-tuple-element.48), channel_id=1, source_target_pairs={{0,8},{8,0},{16,24},{24,16},{1,9},{9,1},{17,25},{25,17},{2,10},{10... | collective-permute-start | bytes 393224 | tf_op jit(solution)/shard_map/ppermute | solution.py:38
  71.1 12.9 %collective-permute-start.26 = (bf16[8,64,128]{2,1,0:T(8,128)(2,1)S(1)}, bf16[8,64,128]{2,1,0:T(8,128)(2,1)S(1)}, u32[]{:S(2)}, u32[]{:S(2)}) collective-permute-start(bf16[8,64,128]{2,1,0:T(8,128)(2,1)S(1)} %get-tuple-element.49), channel_id=1, source_target_pairs={{0,16},{8,24},{16,0},{24,8},{1,17},{9,25},{17,1},{25,9},{2,18},{10... | collective-permute-start | bytes 393224 | tf_op jit(solution)/shard_map/ppermute | solution.py:38
  73.3 10.8 %collective-permute-start.27 = (bf16[8,64,128]{2,1,0:T(8,128)(2,1)S(1)}, bf16[8,64,128]{2,1,0:T(8,128)(2,1)S(1)}, u32[]{:S(2)}, u32[]{:S(2)}) collective-permute-start(bf16[8,64,128]{2,1,0:T(8,128)(2,1)S(1)} %get-tuple-element.50), channel_id=1, source_target_pairs={{0,24},{8,16},{16,8},{24,0},{1,25},{9,17},{17,9},{25,1},{2,26},{10... | collective-permute-start | bytes 393224 | tf_op jit(solution)/shard_map/ppermute | solution.py:38
  75.6 8.5 %collective-permute-start.22 = (bf16[8,64,128]{2,1,0:T(8,128)(2,1)S(1)}, bf16[8,64,128]{2,1,0:T(8,128)(2,1)S(1)}, u32[]{:S(2)}, u32[]{:S(2)}) collective-permute-start(bf16[8,64,128]{2,1,0:T(8,128)(2,1)S(1)} %get-tuple-element.45), channel_id=1, source_target_pairs={{0,2},{1,3},{2,0},{3,1},{4,6},{5,7},{6,4},{7,5},{8,10},{9,11},{10,... | collective-permute-start | bytes 393224 | tf_op jit(solution)/shard_map/ppermute | solution.py:38
  77.1 7.8 %collective-permute-start.23 = (bf16[8,64,128]{2,1,0:T(8,128)(2,1)S(1)}, bf16[8,64,128]{2,1,0:T(8,128)(2,1)S(1)}, u32[]{:S(2)}, u32[]{:S(2)}) collective-permute-start(bf16[8,64,128]{2,1,0:T(8,128)(2,1)S(1)} %get-tuple-element.46), channel_id=1, source_target_pairs={{0,4},{1,5},{2,6},{3,7},{4,0},{5,1},{6,2},{7,3},{8,12},{9,13},{10,... | collective-permute-start | bytes 393224 | tf_op jit(solution)/shard_map/ppermute | solution.py:38
  78.8 6.1 %collective-permute-start.24 = (bf16[8,64,128]{2,1,0:T(8,128)(2,1)S(1)}, bf16[8,64,128]{2,1,0:T(8,128)(2,1)S(1)}, u32[]{:S(2)}, u32[]{:S(2)}) collective-permute-start(bf16[8,64,128]{2,1,0:T(8,128)(2,1)S(1)} %get-tuple-element.47), channel_id=1, source_target_pairs={{0,6},{1,7},{2,4},{3,5},{4,2},{5,3},{6,0},{7,1},{8,14},{9,15},{10,... | collective-permute-start | bytes 393224 | tf_op jit(solution)/shard_map/ppermute | solution.py:38
  85.7 6.6 %collective-permute-start.30 = (bf16[8,64,128]{2,1,0:T(8,128)(2,1)S(1)}, bf16[8,64,128]{2,1,0:T(8,128)(2,1)S(1)}, u32[]{:S(2)}, u32[]{:S(2)}) collective-permute-start(bf16[8,64,128]{2,1,0:T(8,128)(2,1)S(1)} %get-tuple-element.52.refs_4_), channel_id=1, source_target_pairs={{0,6},{1,7},{2,4},{3,5},{4,2},{5,3},{6,0},{7,1},{8,14},{9,15},{10,... | collective-permute-start | bytes 393224 | tf_op jit(solution)/shard_map/ppermute | solution.py:38
  87.1 6.4 %collective-permute-start.29 = (bf16[8,64,128]{2,1,0:T(8,128)(2,1)S(1)}, bf16[8,64,128]{2,1,0:T(8,128)(2,1)S(1)}, u32[]{:S(2)}, u32[]{:S(2)}) collective-permute-start(bf16[8,64,128]{2,1,0:T(8,128)(2,1)S(1)} %get-tuple-element.52.refs_4_), channel_id=1, source_target_pairs={{0,4},{1,5},{2,6},{3,7},{4,0},{5,1},{6,2},{7,3},{8,12},{9,13},{10,... | collective-permute-start | bytes 393224 | tf_op jit(solution)/shard_map/ppermute | solution.py:38
  88.4 5.1 %collective-permute-start.28 = (bf16[8,64,128]{2,1,0:T(8,128)(2,1)S(1)}, bf16[8,64,128]{2,1,0:T(8,128)(2,1)S(1)}, u32[]{:S(2)}, u32[]{:S(2)}) collective-permute-start(bf16[8,64,128]{2,1,0:T(8,128)(2,1)S(1)} %get-tuple-element.52.refs_4_), channel_id=1, source_target_pairs={{0,2},{1,3},{2,0},{3,1},{4,6},{5,7},{6,4},{7,5},{8,10},{9,11},{10,... | collective-permute-start | bytes 393224 | tf_op jit(solution)/shard_map/ppermute | solution.py:38
  93.6 4.5 %collective-permute-start.31 = (bf16[4,8,64,128]{3,2,1,0:T(8,128)(2,1)S(1)}, bf16[4,8,64,128]{3,2,1,0:T(8,128)(2,1)S(1)}, u32[]{:S(2)}, u32[]{:S(2)}) collective-permute-start(bf16[4,8,64,128]{3,2,1,0:T(8,128)(2,1)S(1)} %pad_maximum_fusion.2.refs_3_), channel_id=1, source_target_pairs={{0,1},{1,0},{2,3},{3,2},{4,5},{5,4},{6,7},{7,6},{8,9},{9,8},{10,11... | collective-permute-start | bytes 1572872 | tf_op jit(solution)/shard_map/ppermute | solution.py:38
  93.7 8.3 %collective-permute-start.34 = (bf16[8,64,128]{2,1,0:T(8,128)(2,1)S(1)}, bf16[8,64,128]{2,1,0:T(8,128)(2,1)S(1)}, u32[]{:S(2)}, u32[]{:S(2)}) collective-permute-start(bf16[8,64,128]{2,1,0:T(8,128)(2,1)S(1)} %get-tuple-element.52.refs_4_), channel_id=1, source_target_pairs={{0,24},{8,16},{16,8},{24,0},{1,25},{9,17},{17,9},{25,1},{2,26},{10... | collective-permute-start | bytes 393224 | tf_op jit(solution)/shard_map/ppermute | solution.py:38
  95.8 14.0 %collective-permute-start.33 = (bf16[8,64,128]{2,1,0:T(8,128)(2,1)S(1)}, bf16[8,64,128]{2,1,0:T(8,128)(2,1)S(1)}, u32[]{:S(2)}, u32[]{:S(2)}) collective-permute-start(bf16[8,64,128]{2,1,0:T(8,128)(2,1)S(1)} %get-tuple-element.52.refs_4_), channel_id=1, source_target_pairs={{0,16},{8,24},{16,0},{24,8},{1,17},{9,25},{17,1},{25,9},{2,18},{10... | collective-permute-start | bytes 393224 | tf_op jit(solution)/shard_map/ppermute | solution.py:38
  98.1 11.7 %collective-permute-start.32 = (bf16[8,64,128]{2,1,0:T(8,128)(2,1)S(1)}, bf16[8,64,128]{2,1,0:T(8,128)(2,1)S(1)}, u32[]{:S(2)}, u32[]{:S(2)}) collective-permute-start(bf16[8,64,128]{2,1,0:T(8,128)(2,1)S(1)} %get-tuple-element.52.refs_4_), channel_id=1, source_target_pairs={{0,8},{8,0},{16,24},{24,16},{1,9},{9,1},{17,25},{25,17},{2,10},{10... | collective-permute-start | bytes 393224 | tf_op jit(solution)/shard_map/ppermute | solution.py:38
  111.1 1.2 collective-permute-start.35
  112.3 4.7 %collective-permute-start.38 = (f32[40,128]{1,0:T(8,128)S(1)}, f32[40,128]{1,0:T(8,128)S(1)}, u32[]{:S(2)}, u32[]{:S(2)}) collective-permute-start(f32[40,128]{1,0:T(8,128)S(1)} %add.12), channel_id=1, source_target_pairs={{0,6},{1,7},{2,4},{3,5},{4,2},{5,3},{6,0},{7,1},{8,14},{9,15},{10,... | collective-permute-start | bytes 61448 | tf_op jit(solution)/shard_map/ppermute | solution.py:38
  113.8 3.8 %collective-permute-start.37 = (f32[40,128]{1,0:T(8,128)S(1)}, f32[40,128]{1,0:T(8,128)S(1)}, u32[]{:S(2)}, u32[]{:S(2)}) collective-permute-start(f32[40,128]{1,0:T(8,128)S(1)} %add.12), channel_id=1, source_target_pairs={{0,4},{1,5},{2,6},{3,7},{4,0},{5,1},{6,2},{7,3},{8,12},{9,13},{10,... | collective-permute-start | bytes 61448 | tf_op jit(solution)/shard_map/ppermute | solution.py:38
  115.1 3.8 %collective-permute-start.36 = (f32[40,128]{1,0:T(8,128)S(1)}, f32[40,128]{1,0:T(8,128)S(1)}, u32[]{:S(2)}, u32[]{:S(2)}) collective-permute-start(f32[40,128]{1,0:T(8,128)S(1)} %add.12), channel_id=1, source_target_pairs={{0,2},{1,3},{2,0},{3,1},{4,6},{5,7},{6,4},{7,5},{8,10},{9,11},{10,... | collective-permute-start | bytes 61448 | tf_op jit(solution)/shard_map/ppermute | solution.py:38
  118.9 5.8 %collective-permute-start.41 = (f32[40,128]{1,0:T(8,128)S(1)}, f32[40,128]{1,0:T(8,128)S(1)}, u32[]{:S(2)}, u32[]{:S(2)}) collective-permute-start(f32[40,128]{1,0:T(8,128)S(1)} %add_add_fusion.refs_1_), channel_id=1, source_target_pairs={{0,24},{8,16},{16,8},{24,0},{1,25},{9,17},{17,9},{25,1},{2,26},{10... | collective-permute-start | bytes 61448 | tf_op jit(solution)/shard_map/ppermute | solution.py:38
  121.1 4.7 %collective-permute-start.40 = (f32[40,128]{1,0:T(8,128)S(1)}, f32[40,128]{1,0:T(8,128)S(1)}, u32[]{:S(2)}, u32[]{:S(2)}) collective-permute-start(f32[40,128]{1,0:T(8,128)S(1)} %add_add_fusion.refs_1_), channel_id=1, source_target_pairs={{0,16},{8,24},{16,0},{24,8},{1,17},{9,25},{17,1},{25,9},{2,18},{10... | collective-permute-start | bytes 61448 | tf_op jit(solution)/shard_map/ppermute | solution.py:38
  121.1 4.7 %collective-permute-start.39 = (f32[40,128]{1,0:T(8,128)S(1)}, f32[40,128]{1,0:T(8,128)S(1)}, u32[]{:S(2)}, u32[]{:S(2)}) collective-permute-start(f32[40,128]{1,0:T(8,128)S(1)} %add_add_fusion.refs_1_), channel_id=1, source_target_pairs={{0,8},{8,0},{16,24},{24,16},{1,9},{9,1},{17,25},{25,17},{2,10},{10... | collective-permute-start | bytes 61448 | tf_op jit(solution)/shard_map/ppermute | solution.py:38

commit v5 on v4

--- a/solution.py
+++ b/solution.py
@@ -16,21 +16,20 @@
 F32 = jnp.float32
 VMEM = pl.BlockSpec(memory_space=pltpu.VMEM)
 SMEM = pl.BlockSpec(memory_space=pltpu.SMEM)
-ANY = pl.BlockSpec(memory_space=pl.ANY)
 DEGREE_ROWS = 16
 
 
-def call(kernel, out_shape, scratch, limit, args, flops=0, smem=0, after=()):
+def call(kernel, out_shape, scratch, limit, args, flops=0, smem=0):
     moved = sum(x.size * x.dtype.itemsize for x in args)
     return pl.pallas_call(
-        lambda *refs: kernel(*refs[len(after) :]),
+        kernel,
         out_shape=out_shape,
-        in_specs=[ANY] * len(after) + [SMEM] * smem + [VMEM] * (len(args) - smem),
+        in_specs=[SMEM] * smem + [VMEM] * (len(args) - smem),
         out_specs=jax.tree.map(lambda _: VMEM, out_shape),
         scratch_shapes=scratch,
         compiler_params=pltpu.CompilerParams(vmem_limit_bytes=limit * 2**20),
         cost_estimate=pl.CostEstimate(flops=flops, bytes_accessed=moved, transcendentals=0),
-    )(*after, *args)
+    )(*args)
 
 
 def trade(part, axis, d):
@@ -39,7 +38,8 @@
 
 
 def exchange(parts, axis, step=1):
-    return [trade(part, axis, step * d) for d, part in enumerate(parts, 1)]
+    far_first = [trade(part, axis, step * d) for d, part in reversed(list(enumerate(parts, 1)))]
+    return far_first[::-1]
 
 
 def tiles_first(ref, width):
@@ -70,6 +70,15 @@
     )
 
 
+def fill(panel, part_refs):
+    place_at = 0
+    for part in part_refs:
+        blocks = part.reshape(-1, *part.shape[-2:])
+        count = blocks.shape[0]
+        panel[place_at : place_at + count, : part.shape[-2], :] = blocks[...]
+        place_at += count
+
+
 def place(tile, group, me, halves):
     apart = (tile // group) ^ me
     if halves:
@@ -77,65 +86,63 @@
     return apart * group + tile % group
 
 
-def product_kernel(parts_n, degree, dims, halves, meta, in_rows, out_rows, tiles_ref, *refs):
-    part_refs, refs = refs[:parts_n], refs[parts_n:]
-    own_ref, send_refs, (panel, total) = refs[0], refs[1:-2], refs[-2:]
-    group, vectors_n, width = own_ref.shape[-3], part_refs[0].shape[-2], own_ref.shape[-1]
-    place_at = 0
-    for part in part_refs:
-        blocks = part.reshape(-1, vectors_n, width)
-        count = blocks.shape[0]
-        panel[place_at : place_at + count, :vectors_n, :] = blocks[...]
-        place_at += count
-    if degree:
-        panel[:, vectors_n:, :] = jnp.ones(
-            (panel.shape[0], panel.shape[1] - vectors_n, width), BF16
-        )
-    total[...] = jnp.zeros_like(total)
+def product_kernel(counts, degree, meta, tile_rows, tile_cols, tiles_ref, *refs):
+    cols_n, rows_n, half = counts
+    col_parts, refs = refs[:cols_n], refs[cols_n:]
+    row_parts, refs = refs[:rows_n], refs[rows_n:]
+    kept_ref, swap_ref, own_ref, *send_refs = refs[:-4]
+    col_panel, row_panel, row_total, col_total = refs[-4:]
+    group, vectors_n, width = col_parts[0].shape
+    for panel, parts in ((col_panel, col_parts), (row_panel, row_parts)):
+        fill(panel, parts)
+        if degree:
+            panel[:, vectors_n:, :] = jnp.ones(
+                (panel.shape[0], panel.shape[1] - vectors_n, width), BF16
+            )
+    row_total[...] = jnp.zeros_like(row_total)
+    col_total[...] = jnp.zeros_like(col_total)
     for t in range(tiles_ref.shape[0]):
-        source = place(in_rows[t], group, meta[0], halves[0])
-        target = place(out_rows[t], group, meta[1], halves[1])
-        total[target] += lax.dot_general(
-            panel[source], tiles_ref[t], dims, preferred_element_type=F32
-        )
-    kept = 1
-    if halves[1]:
-        kept = halves[1]
-        for d in range(kept):
-            own_ref[d] = total[d * group : (d + 1) * group]
-        sends = [send_refs[0].at[d] for d in range(kept)]
-    else:
-        own_ref[...] = total[:group]
-        sends = send_refs
-    for d, send in enumerate(sends, kept):
+        tile = tiles_ref[t]
+        row, col = tile_rows[t], tile_cols[t]
+        here = place(col, group, meta[0], 0)
+        row_total[place(row, group, meta[1], half)] += lax.dot_general(
+            col_panel[here], tile, NT, preferred_element_type=F32
+        )
+        col_total[here] += lax.dot_general(
+            row_panel[place(row, group, meta[1], 0)], tile, NN, preferred_element_type=F32
+        )
+    for d in range(half):
+        kept_ref[d] = row_total[d * group : (d + 1) * group]
+    own_ref[...] = col_total[:group]
+    sends = [(row_total, half + d, swap_ref.at[d]) for d in range(half)]
+    sends += [(col_total, d, send) for d, send in enumerate(send_refs, 1)]
+    for total, d, send in sends:
         send[:group] = total[d * group : (d + 1) * group, :vectors_n, :].astype(BF16)
         if degree:
             send[group] = split_degree(degree_of(total, d * group, group, vectors_n), vectors_n)
 
 
-def products(tiles, in_rows, out_rows, meta, parts, group, out_n, dims, halves, degree, after=()):
-    vectors_n, width = parts[0].shape[-2:]
+def products(tiles, tile_rows, tile_cols, meta, col_parts, row_parts, degree):
+    group, vectors_n, width = col_parts[0].shape
+    rows_n, half = len(col_parts), len(row_parts)
     height = vectors_n + (DEGREE_ROWS if degree else 0)
     blocks = group + (1 if degree else 0)
-    half = halves[1]
-    if half:
-        out_shape = [
-            jax.ShapeDtypeStruct((half, group, height, width), F32),
-            jax.ShapeDtypeStruct((half, blocks, vectors_n, width), BF16),
-        ]
-    else:
-        out_shape = [jax.ShapeDtypeStruct((group, height, width), F32)]
-        out_shape += [jax.ShapeDtypeStruct((blocks, vectors_n, width), BF16)] * (out_n - 1)
-    in_blocks = sum(part.size for part in parts) // (vectors_n * width)
+    out_shape = [
+        jax.ShapeDtypeStruct((half, group, height, width), F32),
+        jax.ShapeDtypeStruct((half, blocks, vectors_n, width), BF16),
+        jax.ShapeDtypeStruct((group, height, width), F32),
+    ]
+    out_shape += [jax.ShapeDtypeStruct((blocks, vectors_n, width), BF16)] * (rows_n - 1)
     scratch = [
-        pltpu.VMEM((in_blocks, height, width), BF16),
-        pltpu.VMEM((out_n * group, height, width), F32),
+        pltpu.VMEM((rows_n * group, height, width), BF16),
+        pltpu.VMEM((2 * half * group, height, width), BF16),
+        pltpu.VMEM((2 * half * group, height, width), F32),
+        pltpu.VMEM((rows_n * group, height, width), F32),
     ]
-    kernel = functools.partial(product_kernel, len(parts), degree, dims, halves)
-    flops = 2 * tiles.size * height
-    args = [meta, in_rows, out_rows, tiles, *parts]
-    own, *send = call(kernel, out_shape, scratch, 24, args, flops, 3, after)
-    return own, send
+    kernel = functools.partial(product_kernel, (rows_n, half, half), degree)
+    args = [meta, tile_rows, tile_cols, tiles, *col_parts, *row_parts]
+    kept, swap, own, *send = call(kernel, out_shape, scratch, 32, args, 4 * tiles.size * height, 3)
+    return kept, swap, own, send
 
 
 def merge_kernel(degree, kept, got, own_ref, *send_refs):
@@ -217,25 +224,22 @@
     )
 
 
-def half_form_kernel(halves, meta, tile_rows, tiles_ref, own_parts, other_parts, out_ref, panel):
-    _, group, vectors_n, width = own_parts.shape
-    for d in range(halves):
-        panel[d * group : (d + 1) * group] = own_parts[d]
-        panel[(halves + d) * group : (halves + d + 1) * group] = other_parts[d]
+def form_kernel(counts, meta, tile_rows, tile_cols, tiles_ref, gram_ref, *refs):
+    cols_n, rows_n = counts
+    col_parts, refs = refs[:cols_n], refs[cols_n:]
+    row_parts, (out_ref, col_panel, row_panel, left, right) = refs[:rows_n], refs[rows_n:]
+    group, vectors_n, width = col_parts[0].shape
+    fill(col_panel, col_parts)
+    fill(row_panel, row_parts)
     for t in range(tiles_ref.shape[0]):
-        row = place(tile_rows[t], group, meta[1], halves)
-        out_ref[:, t * width : (t + 1) * width] = lax.dot_general(
-            panel[row], tiles_ref[t], NN, preferred_element_type=F32
+        columns = slice(t * width, (t + 1) * width)
+        left[:, columns] = row_panel[place(tile_rows[t], group, meta[1], 0)]
+        right[:, columns] = lax.dot_general(
+            col_panel[place(tile_cols[t], group, meta[0], 0)],
+            tiles_ref[t],
+            NT,
+            preferred_element_type=F32,
         ).astype(BF16)
-
-
-def form_kernel(parts_n, meta, tile_cols, left, gram_ref, *refs):
-    part_refs, (out_ref, panel, right) = refs[:parts_n], refs[parts_n:]
-    group, vectors_n, width = part_refs[0].shape
-    for d, part in enumerate(part_refs):
-        panel[d * group : (d + 1) * group] = part[...]
-    for t in range(right.shape[1] // width):
-        right[:, t * width : (t + 1) * width] = panel[place(tile_cols[t], group, meta[0], 0)]
     form = lax.dot_general(left[...], right[...], NT, preferred_element_type=F32)
     swapped = lax.dot_general(right[...], left[...], NT, preferred_element_type=F32)
     projected = gram_ref[:, vectors_n:] - 0.5 * (form + swapped)
@@ -310,7 +314,6 @@
     group = own_nodes // width
     row_me, col_me = lax.axis_index("row"), lax.axis_index("col")
     meta = jnp.stack([row_me, col_me]).astype(jnp.int32)
-    swapped = jnp.stack([col_me, row_me]).astype(jnp.int32)
 
     rounded_shape = jax.ShapeDtypeStruct((group, vectors_n, width), BF16)
     vector_shape = jax.ShapeDtypeStruct((vectors_n, own_nodes), F32)
@@ -318,29 +321,16 @@
     chips_n = cols_n // 2
 
     def gather(rounded):
-        chips = jnp.stack([rounded, *exchange([rounded] * (chips_n - 1), "col", 2)])
         col_parts = [rounded, *exchange([rounded] * (rows_n - 1), "row")]
-        return col_parts, [chips, trade(chips, "col", 1)]
+        pair = jnp.stack([rounded, trade(rounded, "col", 1)])
+        return col_parts, [pair, *exchange([pair] * (chips_n - 1), "col", 2)]
 
     def apply(rounded, degree):
         col_parts, row_parts = gather(rounded)
-        col_own, col_send = products(
-            tiles, tile_rows, tile_cols, swapped, row_parts, group, rows_n, NN, (chips_n, 0), degree
+        kept, send, col_own, col_send = products(
+            tiles, tile_rows, tile_cols, meta, col_parts, row_parts, degree
         )
         col_got = exchange(col_send, "row")
-        kept, (send,) = products(
-            tiles,
-            tile_cols,
-            tile_rows,
-            meta,
-            col_parts,
-            group,
-            cols_n,
-            NT,
-            (0, chips_n),
-            degree,
-            [col_own],
-        )
         row_own, row_send = merge(kept, trade(send, "col", 1), degree)
         row_got = exchange(row_send, "col", 2)
         return [row_own, col_own, *row_got, *col_got]
@@ -364,23 +354,19 @@
     )
     col_parts, row_parts = gather(rounded)
     spread = (vectors_n, tiles.shape[0] * width)
-    left = call(
-        functools.partial(half_form_kernel, chips_n),
-        jax.ShapeDtypeStruct(spread, BF16),
-        [pltpu.VMEM((cols_n * group, vectors_n, width), BF16)],
+    sums = call(
+        functools.partial(form_kernel, (len(col_parts), len(row_parts))),
+        jax.ShapeDtypeStruct((vectors_n // 2 + 8, 2 * vectors_n), F32),
+        [
+            pltpu.VMEM((rows_n * group, vectors_n, width), BF16),
+            pltpu.VMEM((cols_n * group, vectors_n, width), BF16),
+            pltpu.VMEM(spread, BF16),
+            pltpu.VMEM(spread, BF16),
+        ],
         24,
-        [meta, tile_rows, tiles, *row_parts],
-        2 * tiles.size * vectors_n,
-        2,
-    )
-    sums = call(
-        functools.partial(form_kernel, rows_n),
-        jax.ShapeDtypeStruct((vectors_n // 2 + 8, 2 * vectors_n), F32),
-        [pltpu.VMEM((rows_n * group, vectors_n, width), BF16), pltpu.VMEM(spread, BF16)],
-        24,
-        [meta, tile_cols, left, gram, *col_parts],
-        4 * vectors_n * tiles.size // width,
-        2,
+        [meta, tile_rows, tile_cols, tiles, gram, *col_parts, *row_parts],
+        4 * tiles.size * vectors_n,
+        3,
     )
     sums = sums + trade(sums, "col", 1)
     sums = tree_sum([sums, *exchange([sums] * (chips_n - 1), "col", 2)])

time: 133 us -> 121 us (0.910)
  waiting for transfers between devices: 63.8 us -> 33.7 us
  starting transfers between devices: 50.1 us -> 67.5 us
  local copies, waits for them, and re-layouts: 0.96 us -> 3.5 us
  Pallas kernels: 16.9 us -> 14.7 us
    ppermute x42, waiting for transfers between devices: 63.8 us -> 33.7 us  [trade(): return lax.ppermute(part, axis, [(i, i ^ d) for i in range(n)])]
    ppermute x42, starting transfers between devices: 50.1 us -> 67.5 us  [trade(): return lax.ppermute(part, axis, [(i, i ^ d) for i in range(n)])]
    unnamed x10 -> x16, local copies, waits for them, and re-layouts: 0.96 us -> 3.5 us
    pallas_call x12 -> x9, Pallas kernels: 16.9 us -> 14.7 us  [call(): pl.pallas_call(kernel, out_shape=out_shape, in_specs=[SMEM] * smem + [VME...]
  transfers between devices with their start and end apart: 42 -> 42, of which waited for: 26 -> 23; matrix products, arithmetic and copies ran while one was open for 0% -> 0% of each run, Pallas kernels for 3% -> 0%
where the time goes in v5:
time: 121 us; the launch traced here: 120 us
  starting transfers between devices  67.5 us (56%)
  waiting for transfers between devices  33.7 us (28%)
  Pallas kernels  14.7 us (12%)
  local copies, waits for them, and re-layouts  3.5 us (3%)
    ppermute x42, starting transfers between devices, trade(): return lax.ppermute(part, axis, [(i, i ^ d) for i in range(n)])  67.5 us
    ppermute x42, waiting for transfers between devices, trade(): return lax.ppermute(part, axis, [(i, i ^ d) for i in range(n)])  33.7 us
    pallas_call x9, Pallas kernels, call(): pl.pallas_call(kernel, out_shape=out_shape, in_specs=[SMEM] * smem + [VME...  14.7 us
    unnamed x16, local copies, waits for them, and re-layouts  3.5 us
  transfers between devices with their start and end apart: 42, of which 23 were waited for; matrix products, arithmetic and copies ran while one was open for 0% of the time, Pallas kernels for 0%

profile of v5, /device:TPU:0, one launch (start us, length us, event | category | flops | bytes accessed | tf_op | source)
XLA Modules:
  0.0 120.4 jit_solution(13700920030503547380)
XLA Ops:
  0.6 0.9 copy-done.2
  2.1 4.7 %collective-permute-start.2 = (bf16[8,64,128]{2,1,0:T(8,128)(2,1)S(1)}, bf16[8,64,128]{2,1,0:T(8,128)(2,1)S(1)}, u32[]{:S(2)}, u32[]{:S(2)}) collective-permute-start(bf16[8,64,128]{2,1,0:T(8,128)(2,1)S(1)} %shard_map.59.refs_0_), channel_id=1, source_target_pairs={{0,24},{8,16},{16,8},{24,0},{1,25},{9,17},{17,9},{25,1},{2,26},{10... | collective-permute-start | bytes 393224 | tf_op jit(solution)/shard_map/ppermute | solution.py:37
  6.8 2.5 %collective-permute-start.6 = (bf16[2,8,64,128]{3,2,1,0:T(8,128)(2,1)S(1)}, bf16[2,8,64,128]{3,2,1,0:T(8,128)(2,1)S(1)}, u32[]{:S(2)}, u32[]{:S(2)}) collective-permute-start(bf16[2,8,64,128]{3,2,1,0:T(8,128)(2,1)S(1)} %pad_maximum_fusion.refs_4_), channel_id=1, source_target_pairs={{0,6},{1,7},{2,4},{3,5},{4,2},{5,3},{6,0},{7,1},{8,14},{9,15},{10,... | collective-permute-start | bytes 786440 | tf_op jit(solution)/shard_map/ppermute | solution.py:37
  11.0 5.7 %collective-permute-start = (bf16[8,64,128]{2,1,0:T(8,128)(2,1)S(1)}, bf16[8,64,128]{2,1,0:T(8,128)(2,1)S(1)}, u32[]{:S(2)}, u32[]{:S(2)}) collective-permute-start(bf16[8,64,128]{2,1,0:T(8,128)(2,1)S(1)} %shard_map.59.refs_0_), channel_id=1, source_target_pairs={{0,8},{8,0},{16,24},{24,16},{1,9},{9,1},{17,25},{25,17},{2,10},{10... | collective-permute-start | bytes 393224 | tf_op jit(solution)/shard_map/ppermute | solution.py:37
  16.8 1.8 %collective-permute-done.1.refs_2_ = bf16[8,64,128]{2,1,0:T(8,128)(2,1)S(1)} collective-permute-done((bf16[8,64,128]{2,1,0:T(8,128)(2,1)S(1)}, bf16[8,64,128]{2,1,0:T(8,128)(2,1)S(1)}, u32[]{:S(2)}, u32[]{:S(2)}) %collective-permute-start.1) | collective-permute-done | bytes 131104 | tf_op jit(solution)/shard_map/ppermute | solution.py:37
  18.6 2.3 %collective-permute-done.refs_1_ = bf16[8,64,128]{2,1,0:T(8,128)(2,1)S(1)} collective-permute-done((bf16[8,64,128]{2,1,0:T(8,128)(2,1)S(1)}, bf16[8,64,128]{2,1,0:T(8,128)(2,1)S(1)}, u32[]{:S(2)}, u32[]{:S(2)}) %collective-permute-start) | collective-permute-done | bytes 131104 | tf_op jit(solution)/shard_map/ppermute | solution.py:37
  21.9 1.2 %copy-done = bf16[1,1,32,128,128]{4,3,2,1,0:T(8,128)(2,1)S(1)} copy-done((bf16[1,1,32,128,128]{4,3,2,1,0:T(8,128)(2,1)S(1)}, bf16[1,1,32,128,128]{4,3,2,1,0:T(8,128)(2,1)}, u32[]{:S(2)}) %copy-start) | copy-done | bytes 1048600
  24.4 2.2 %shard_map.60 = (f32[4,8,80,128]{3,2,1,0:T(8,128)S(1)}, bf16[4,9,64,128]{3,2,1,0:T(8,128)(2,1)S(1)}, f32[8,80,128]{2,1,0:T(8,128)S(1)}, bf16[9,64,128]{2,1,0:T(8...) custom-call(s32[2]{0:T(128)S(1)} %pad_add_fusion.meta, s32[32]{0:T(128)S(1)} %bitcast.17, ...), custom_call_target="tpu_custom_call" | custom-call | flops 167772160 | bytes 2621704 | tf_op jit(solution)/shard_map/pallas_call | solution.py:24
  26.8 2.4 %collective-permute-start.12 = (bf16[9,64,128]{2,1,0:T(8,128)(2,1)S(1)}, bf16[9,64,128]{2,1,0:T(8,128)(2,1)S(1)}, u32[]{:S(2)}, u32[]{:S(2)}) collective-permute-start(bf16[9,64,128]{2,1,0:T(8,128)(2,1)S(1)} %get-tuple-element.36), channel_id=1, source_target_pairs={{0,16},{8,24},{16,0},{24,8},{1,17},{9,25},{17,1},{25,9},{2,18},{10... | collective-permute-start | bytes 442376 | tf_op jit(solution)/shard_map/ppermute | solution.py:37
  29.2 1.9 %collective-permute-start.13 = (bf16[9,64,128]{2,1,0:T(8,128)(2,1)S(1)}, bf16[9,64,128]{2,1,0:T(8,128)(2,1)S(1)}, u32[]{:S(2)}, u32[]{:S(2)}) collective-permute-start(bf16[9,64,128]{2,1,0:T(8,128)(2,1)S(1)} %get-tuple-element.37), channel_id=1, source_target_pairs={{0,24},{8,16},{16,8},{24,0},{1,25},{9,17},{17,9},{25,1},{2,26},{10... | collective-permute-start | bytes 442376 | tf_op jit(solution)/shard_map/ppermute | solution.py:37
  31.3 1.6 %collective-permute-start.8 = (bf16[9,64,128]{2,1,0:T(8,128)(2,1)S(1)}, bf16[9,64,128]{2,1,0:T(8,128)(2,1)S(1)}, u32[]{:S(2)}, u32[]{:S(2)}) collective-permute-start(bf16[9,64,128]{2,1,0:T(8,128)(2,1)S(1)} %get-tuple-element.32), channel_id=1, source_target_pairs={{0,2},{1,3},{2,0},{3,1},{4,6},{5,7},{6,4},{7,5},{8,10},{9,11},{10,... | collective-permute-start | bytes 442376 | tf_op jit(solution)/shard_map/ppermute | solution.py:37
  33.6 1.9 %collective-permute-done.11.refs_3_ = bf16[9,64,128]{2,1,0:T(8,128)(2,1)S(1)} collective-permute-done((bf16[9,64,128]{2,1,0:T(8,128)(2,1)S(1)}, bf16[9,64,128]{2,1,0:T(8,128)(2,1)S(1)}, u32[]{:S(2)}, u32[]{:S(2)}) %collective-permute-start.11) | collective-permute-done | bytes 147488 | tf_op jit(solution)/shard_map/ppermute | solution.py:37
  35.5 1.8 %collective-permute-start.10 = (bf16[9,64,128]{2,1,0:T(8,128)(2,1)S(1)}, bf16[9,64,128]{2,1,0:T(8,128)(2,1)S(1)}, u32[]{:S(2)}, u32[]{:S(2)}) collective-permute-start(bf16[9,64,128]{2,1,0:T(8,128)(2,1)S(1)} %get-tuple-element.34), channel_id=1, source_target_pairs={{0,6},{1,7},{2,4},{3,5},{4,2},{5,3},{6,0},{7,1},{8,14},{9,15},{10,... | collective-permute-start | bytes 442376 | tf_op jit(solution)/shard_map/ppermute | solution.py:37
  37.3 3.4 %collective-permute-done.12.refs_4_ = bf16[9,64,128]{2,1,0:T(8,128)(2,1)S(1)} collective-permute-done((bf16[9,64,128]{2,1,0:T(8,128)(2,1)S(1)}, bf16[9,64,128]{2,1,0:T(8,128)(2,1)S(1)}, u32[]{:S(2)}, u32[]{:S(2)}) %collective-permute-start.12) | collective-permute-done | bytes 147488 | tf_op jit(solution)/shard_map/ppermute | solution.py:37
  40.8 1.1 collective-permute-done.10.refs_2_
  42.1 1.8 %collective-permute-start.16 = (bf16[8,64,128]{2,1,0:T(8,128)(2,1)S(1)}, bf16[8,64,128]{2,1,0:T(8,128)(2,1)S(1)}, u32[]{:S(2)}, u32[]{:S(2)}) collective-permute-start(bf16[8,64,128]{2,1,0:T(8,128)(2,1)S(1)} %get-tuple-element.40.refs_0_), channel_id=1, source_target_pairs={{0,24},{8,16},{16,8},{24,0},{1,25},{9,17},{17,9},{25,1},{2,26},{10... | collective-permute-start | bytes 393224 | tf_op jit(solution)/shard_map/ppermute | solution.py:37
  43.9 2.0 %collective-permute-start.20 = (bf16[2,8,64,128]{3,2,1,0:T(8,128)(2,1)S(1)}, bf16[2,8,64,128]{3,2,1,0:T(8,128)(2,1)S(1)}, u32[]{:S(2)}, u32[]{:S(2)}) collective-permute-start(bf16[2,8,64,128]{3,2,1,0:T(8,128)(2,1)S(1)} %pad_maximum_fusion.1.refs_4_), channel_id=1, source_target_pairs={{0,6},{1,7},{2,4},{3,5},{4,2},{5,3},{6,0},{7,1},{8,14},{9,15},{10,... | collective-permute-start | bytes 786440 | tf_op jit(solution)/shard_map/ppermute | solution.py:37
  46.0 1.0 collective-permute-start.19
  47.5 2.2 %collective-permute-start.15 = (bf16[8,64,128]{2,1,0:T(8,128)(2,1)S(1)}, bf16[8,64,128]{2,1,0:T(8,128)(2,1)S(1)}, u32[]{:S(2)}, u32[]{:S(2)}) collective-permute-start(bf16[8,64,128]{2,1,0:T(8,128)(2,1)S(1)} %get-tuple-element.40.refs_0_), channel_id=1, source_target_pairs={{0,16},{8,24},{16,0},{24,8},{1,17},{9,25},{17,1},{25,9},{2,18},{10... | collective-permute-start | bytes 393224 | tf_op jit(solution)/shard_map/ppermute | solution.py:37
  49.9 6.2 %collective-permute-start.14 = (bf16[8,64,128]{2,1,0:T(8,128)(2,1)S(1)}, bf16[8,64,128]{2,1,0:T(8,128)(2,1)S(1)}, u32[]{:S(2)}, u32[]{:S(2)}) collective-permute-start(bf16[8,64,128]{2,1,0:T(8,128)(2,1)S(1)} %get-tuple-element.40.refs_0_), channel_id=1, source_target_pairs={{0,8},{8,0},{16,24},{24,16},{1,9},{9,1},{17,25},{25,17},{2,10},{10... | collective-permute-start | bytes 393224 | tf_op jit(solution)/shard_map/ppermute | solution.py:37
  56.1 2.0 %collective-permute-done.15.refs_2_ = bf16[8,64,128]{2,1,0:T(8,128)(2,1)S(1)} collective-permute-done((bf16[8,64,128]{2,1,0:T(8,128)(2,1)S(1)}, bf16[8,64,128]{2,1,0:T(8,128)(2,1)S(1)}, u32[]{:S(2)}, u32[]{:S(2)}) %collective-permute-start.15) | collective-permute-done | bytes 131104 | tf_op jit(solution)/shard_map/ppermute | solution.py:37
  58.1 2.7 %collective-permute-done.14.refs_1_ = bf16[8,64,128]{2,1,0:T(8,128)(2,1)S(1)} collective-permute-done((bf16[8,64,128]{2,1,0:T(8,128)(2,1)S(1)}, bf16[8,64,128]{2,1,0:T(8,128)(2,1)S(1)}, u32[]{:S(2)}, u32[]{:S(2)}) %collective-permute-start.14) | collective-permute-done | bytes 131104 | tf_op jit(solution)/shard_map/ppermute | solution.py:37
  60.9 1.9 %shard_map.63 = (f32[4,8,64,128]{3,2,1,0:T(8,128)S(1)}, bf16[4,8,64,128]{3,2,1,0:T(8,128)(2,1)S(1)}, f32[8,64,128]{2,1,0:T(8,128)S(1)}, bf16[8,64,128]{2,1,0:T(8...) custom-call(s32[2]{0:T(128)S(1)} %pad_add_fusion.meta, s32[32]{0:T(128)S(1)} %bitcast.18, ...), custom_call_target="tpu_custom_call" | custom-call | flops 134217728 | bytes 2621704 | tf_op jit(solution)/shard_map/pallas_call | solution.py:24
  63.1 2.3 %collective-permute-start.26 = (bf16[8,64,128]{2,1,0:T(8,128)(2,1)S(1)}, bf16[8,64,128]{2,1,0:T(8,128)(2,1)S(1)}, u32[]{:S(2)}, u32[]{:S(2)}) collective-permute-start(bf16[8,64,128]{2,1,0:T(8,128)(2,1)S(1)} %get-tuple-element.49), channel_id=1, source_target_pairs={{0,16},{8,24},{16,0},{24,8},{1,17},{9,25},{17,1},{25,9},{2,18},{10... | collective-permute-start | bytes 393224 | tf_op jit(solution)/shard_map/ppermute | solution.py:37
  65.4 1.9 %collective-permute-start.27 = (bf16[8,64,128]{2,1,0:T(8,128)(2,1)S(1)}, bf16[8,64,128]{2,1,0:T(8,128)(2,1)S(1)}, u32[]{:S(2)}, u32[]{:S(2)}) collective-permute-start(bf16[8,64,128]{2,1,0:T(8,128)(2,1)S(1)} %get-tuple-element.50), channel_id=1, source_target_pairs={{0,24},{8,16},{16,8},{24,0},{1,25},{9,17},{17,9},{25,1},{2,26},{10... | collective-permute-start | bytes 393224 | tf_op jit(solution)/shard_map/ppermute | solution.py:37
  67.4 1.6 %collective-permute-start.22 = (bf16[8,64,128]{2,1,0:T(8,128)(2,1)S(1)}, bf16[8,64,128]{2,1,0:T(8,128)(2,1)S(1)}, u32[]{:S(2)}, u32[]{:S(2)}) collective-permute-start(bf16[8,64,128]{2,1,0:T(8,128)(2,1)S(1)} %get-tuple-element.45), channel_id=1, source_target_pairs={{0,2},{1,3},{2,0},{3,1},{4,6},{5,7},{6,4},{7,5},{8,10},{9,11},{10,... | collective-permute-start | bytes 393224 | tf_op jit(solution)/shard_map/ppermute | solution.py:37
  69.0 1.0 collective-permute-start.23
  70.9 1.9 %collective-permute-start.24 = (bf16[8,64,128]{2,1,0:T(8,128)(2,1)S(1)}, bf16[8,64,128]{2,1,0:T(8,128)(2,1)S(1)}, u32[]{:S(2)}, u32[]{:S(2)}) collective-permute-start(bf16[8,64,128]{2,1,0:T(8,128)(2,1)S(1)} %get-tuple-element.47), channel_id=1, source_target_pairs={{0,6},{1,7},{2,4},{3,5},{4,2},{5,3},{6,0},{7,1},{8,14},{9,15},{10,... | collective-permute-start | bytes 393224 | tf_op jit(solution)/shard_map/ppermute | solution.py:37
  72.9 3.2 %collective-permute-done.26.refs_4_ = bf16[8,64,128]{2,1,0:T(8,128)(2,1)S(1)} collective-permute-done((bf16[8,64,128]{2,1,0:T(8,128)(2,1)S(1)}, bf16[8,64,128]{2,1,0:T(8,128)(2,1)S(1)}, u32[]{:S(2)}, u32[]{:S(2)}) %collective-permute-start.26) | collective-permute-done | bytes 131104 | tf_op jit(solution)/shard_map/ppermute | solution.py:37
  77.7 1.9 %collective-permute-start.30 = (bf16[8,64,128]{2,1,0:T(8,128)(2,1)S(1)}, bf16[8,64,128]{2,1,0:T(8,128)(2,1)S(1)}, u32[]{:S(2)}, u32[]{:S(2)}) collective-permute-start(bf16[8,64,128]{2,1,0:T(8,128)(2,1)S(1)} %get-tuple-element.53.refs_0_), channel_id=1, source_target_pairs={{0,24},{8,16},{16,8},{24,0},{1,25},{9,17},{17,9},{25,1},{2,26},{10... | collective-permute-start | bytes 393224 | tf_op jit(solution)/shard_map/ppermute | solution.py:37
  79.6 2.0 %collective-permute-start.34 = (bf16[2,8,64,128]{3,2,1,0:T(8,128)(2,1)S(1)}, bf16[2,8,64,128]{3,2,1,0:T(8,128)(2,1)S(1)}, u32[]{:S(2)}, u32[]{:S(2)}) collective-permute-start(bf16[2,8,64,128]{3,2,1,0:T(8,128)(2,1)S(1)} %pad_maximum_fusion.2.refs_4_), channel_id=1, source_target_pairs={{0,6},{1,7},{2,4},{3,5},{4,2},{5,3},{6,0},{7,1},{8,14},{9,15},{10,... | collective-permute-start | bytes 786440 | tf_op jit(solution)/shard_map/ppermute | solution.py:37
  81.6 0.9 collective-permute-start.33
  83.2 1.9 %collective-permute-start.29 = (bf16[8,64,128]{2,1,0:T(8,128)(2,1)S(1)}, bf16[8,64,128]{2,1,0:T(8,128)(2,1)S(1)}, u32[]{:S(2)}, u32[]{:S(2)}) collective-permute-start(bf16[8,64,128]{2,1,0:T(8,128)(2,1)S(1)} %get-tuple-element.53.refs_0_), channel_id=1, source_target_pairs={{0,16},{8,24},{16,0},{24,8},{1,17},{9,25},{17,1},{25,9},{2,18},{10... | collective-permute-start | bytes 393224 | tf_op jit(solution)/shard_map/ppermute | solution.py:37
  85.6 5.9 %collective-permute-start.28 = (bf16[8,64,128]{2,1,0:T(8,128)(2,1)S(1)}, bf16[8,64,128]{2,1,0:T(8,128)(2,1)S(1)}, u32[]{:S(2)}, u32[]{:S(2)}) collective-permute-start(bf16[8,64,128]{2,1,0:T(8,128)(2,1)S(1)} %get-tuple-element.53.refs_0_), channel_id=1, source_target_pairs={{0,8},{8,0},{16,24},{24,16},{1,9},{9,1},{17,25},{25,17},{2,10},{10... | collective-permute-start | bytes 393224 | tf_op jit(solution)/shard_map/ppermute | solution.py:37
  91.5 1.9 %collective-permute-done.29.refs_2_ = bf16[8,64,128]{2,1,0:T(8,128)(2,1)S(1)} collective-permute-done((bf16[8,64,128]{2,1,0:T(8,128)(2,1)S(1)}, bf16[8,64,128]{2,1,0:T(8,128)(2,1)S(1)}, u32[]{:S(2)}, u32[]{:S(2)}) %collective-permute-start.29) | collective-permute-done | bytes 131104 | tf_op jit(solution)/shard_map/ppermute | solution.py:37
  93.4 2.7 %collective-permute-done.28.refs_1_ = bf16[8,64,128]{2,1,0:T(8,128)(2,1)S(1)} collective-permute-done((bf16[8,64,128]{2,1,0:T(8,128)(2,1)S(1)}, bf16[8,64,128]{2,1,0:T(8,128)(2,1)S(1)}, u32[]{:S(2)}, u32[]{:S(2)}) %collective-permute-start.28) | collective-permute-done | bytes 131104 | tf_op jit(solution)/shard_map/ppermute | solution.py:37
  96.1 2.3 %shard_map.66 = f32[40,128]{1,0:T(8,128)S(1)} custom-call(s32[2]{0:T(128)S(1)} %pad_add_fusion.meta, s32[32]{0:T(128)S(1)} %bitcast.19, s32[32]{0:T(128)S(1)} %bitcast.22, bf16[32,128,128]{2,1,0:T(8,128)(2,1)S(1)} %bitcast.13, f32[64,128]{1,0:T(8,128)S(1)} %get-tuple-element.52.gram_ref, bf16[8,64,128]{2,1,0:T(8,128)(2,1)S(1)} %get-tuple-element.53.refs_0_, ...), custom_call_target="tpu_custom_call" | custom-call | flops 134217728 | bytes 2654472 | tf_op jit(solution)/shard_map/pallas_call | solution.py:24
  98.4 1.2 collective-permute-done.35
  99.6 2.0 %collective-permute-start.38 = (f32[40,128]{1,0:T(8,128)S(1)}, f32[40,128]{1,0:T(8,128)S(1)}, u32[]{:S(2)}, u32[]{:S(2)}) collective-permute-start(f32[40,128]{1,0:T(8,128)S(1)} %add.12), channel_id=1, source_target_pairs={{0,6},{1,7},{2,4},{3,5},{4,2},{5,3},{6,0},{7,1},{8,14},{9,15},{10,... | collective-permute-start | bytes 61448 | tf_op jit(solution)/shard_map/ppermute | solution.py:37
  101.6 0.9 collective-permute-start.37
  103.1 1.2 collective-permute-done.38
  104.3 1.1 collective-permute-done.37
  105.4 0.9 collective-permute-done.36
  106.4 2.2 %collective-permute-start.41 = (f32[40,128]{1,0:T(8,128)S(1)}, f32[40,128]{1,0:T(8,128)S(1)}, u32[]{:S(2)}, u32[]{:S(2)}) collective-permute-start(f32[40,128]{1,0:T(8,128)S(1)} %add_add_fusion.refs_0_), channel_id=1, source_target_pairs={{0,24},{8,16},{16,8},{24,0},{1,25},{9,17},{17,9},{25,1},{2,26},{10... | collective-permute-start | bytes 61448 | tf_op jit(solution)/shard_map/ppermute | solution.py:37
  108.5 2.3 %collective-permute-start.39 = (f32[40,128]{1,0:T(8,128)S(1)}, f32[40,128]{1,0:T(8,128)S(1)}, u32[]{:S(2)}, u32[]{:S(2)}) collective-permute-start(f32[40,128]{1,0:T(8,128)S(1)} %add_add_fusion.refs_0_), channel_id=1, source_target_pairs={{0,8},{8,0},{16,24},{24,16},{1,9},{9,1},{17,25},{25,17},{2,10},{10... | collective-permute-start | bytes 61448 | tf_op jit(solution)/shard_map/ppermute | solution.py:37
  110.8 1.2 collective-permute-done.41.refs_3_
  112.0 1.2 collective-permute-done.40.refs_2_
  113.2 7.2 %shard_map.67 = (f32[64,1024]{1,0:T(8,128)}, f32[64,64]{1,0:T(8,128)}) custom-call(f32[64,1024]{1,0:T(8,128)S(1)} %get-tuple-element.51.filtered_ref, f32[40,128]{1,0:T(8,128)S(1)} %add_add_fusion.refs_0_, f32[40,128]{1,0:T(8,128)S(1)} %collective-permute-done.39.refs_1_, f32[40,128]{1,0:T(8,128)S(1)} %collective-permute-done.40.refs_2_, ...), custom_call_target="tpu_custom_call" | custom-call | bytes 344064 | tf_op jit(solution)/shard_map/pallas_call | solution.py:24
  (67 shorter events, 11.4 us)
Async XLA Ops:
  0.6 1.0 copy-start.2
  1.6 5.2 %collective-permute-start.3 = (bf16[8,64,128]{2,1,0:T(8,128)(2,1)S(1)}, bf16[8,64,128]{2,1,0:T(8,128)(2,1)S(1)}, u32[]{:S(2)}, u32[]{:S(2)}) collective-permute-start(bf16[8,64,128]{2,1,0:T(8,128)(2,1)S(1)} %shard_map.59.refs_0_), channel_id=1, source_target_pairs={{0,1},{1,0},{2,3},{3,2},{4,5},{5,4},{6,7},{7,6},{8,9},{9,8},{10,11... | collective-permute-start | bytes 393224 | tf_op jit(solution)/shard_map/ppermute | solution.py:37
  2.1 8.9 %collective-permute-start.2 = (bf16[8,64,128]{2,1,0:T(8,128)(2,1)S(1)}, bf16[8,64,128]{2,1,0:T(8,128)(2,1)S(1)}, u32[]{:S(2)}, u32[]{:S(2)}) collective-permute-start(bf16[8,64,128]{2,1,0:T(8,128)(2,1)S(1)} %shard_map.59.refs_0_), channel_id=1, source_target_pairs={{0,24},{8,16},{16,8},{24,0},{1,25},{9,17},{17,9},{25,1},{2,26},{10... | collective-permute-start | bytes 393224 | tf_op jit(solution)/shard_map/ppermute | solution.py:37
  6.8 14.1 %collective-permute-start.6 = (bf16[2,8,64,128]{3,2,1,0:T(8,128)(2,1)S(1)}, bf16[2,8,64,128]{3,2,1,0:T(8,128)(2,1)S(1)}, u32[]{:S(2)}, u32[]{:S(2)}) collective-permute-start(bf16[2,8,64,128]{3,2,1,0:T(8,128)(2,1)S(1)} %pad_maximum_fusion.refs_4_), channel_id=1, source_target_pairs={{0,6},{1,7},{2,4},{3,5},{4,2},{5,3},{6,0},{7,1},{8,14},{9,15},{10,... | collective-permute-start | bytes 786440 | tf_op jit(solution)/shard_map/ppermute | solution.py:37
  9.3 12.4 %collective-permute-start.5 = (bf16[2,8,64,128]{3,2,1,0:T(8,128)(2,1)S(1)}, bf16[2,8,64,128]{3,2,1,0:T(8,128)(2,1)S(1)}, u32[]{:S(2)}, u32[]{:S(2)}) collective-permute-start(bf16[2,8,64,128]{3,2,1,0:T(8,128)(2,1)S(1)} %pad_maximum_fusion.refs_4_), channel_id=1, source_target_pairs={{0,4},{1,5},{2,6},{3,7},{4,0},{5,1},{6,2},{7,3},{8,12},{9,13},{10,... | collective-permute-start | bytes 786440 | tf_op jit(solution)/shard_map/ppermute | solution.py:37
  9.8 12.0 %collective-permute-start.4 = (bf16[2,8,64,128]{3,2,1,0:T(8,128)(2,1)S(1)}, bf16[2,8,64,128]{3,2,1,0:T(8,128)(2,1)S(1)}, u32[]{:S(2)}, u32[]{:S(2)}) collective-permute-start(bf16[2,8,64,128]{3,2,1,0:T(8,128)(2,1)S(1)} %pad_maximum_fusion.refs_4_), channel_id=1, source_target_pairs={{0,2},{1,3},{2,0},{3,1},{4,6},{5,7},{6,4},{7,5},{8,10},{9,11},{10,... | collective-permute-start | bytes 786440 | tf_op jit(solution)/shard_map/ppermute | solution.py:37
  10.4 8.2 %collective-permute-start.1 = (bf16[8,64,128]{2,1,0:T(8,128)(2,1)S(1)}, bf16[8,64,128]{2,1,0:T(8,128)(2,1)S(1)}, u32[]{:S(2)}, u32[]{:S(2)}) collective-permute-start(bf16[8,64,128]{2,1,0:T(8,128)(2,1)S(1)} %shard_map.59.refs_0_), channel_id=1, source_target_pairs={{0,16},{8,24},{16,0},{24,8},{1,17},{9,25},{17,1},{25,9},{2,18},{10... | collective-permute-start | bytes 393224 | tf_op jit(solution)/shard_map/ppermute | solution.py:37
  11.0 9.9 %collective-permute-start = (bf16[8,64,128]{2,1,0:T(8,128)(2,1)S(1)}, bf16[8,64,128]{2,1,0:T(8,128)(2,1)S(1)}, u32[]{:S(2)}, u32[]{:S(2)}) collective-permute-start(bf16[8,64,128]{2,1,0:T(8,128)(2,1)S(1)} %shard_map.59.refs_0_), channel_id=1, source_target_pairs={{0,8},{8,0},{16,24},{24,16},{1,9},{9,1},{17,25},{25,17},{2,10},{10... | collective-permute-start | bytes 393224 | tf_op jit(solution)/shard_map/ppermute | solution.py:37
  21.9 1.2 %copy-start = (bf16[1,1,32,128,128]{4,3,2,1,0:T(8,128)(2,1)S(1)}, bf16[1,1,32,128,128]{4,3,2,1,0:T(8,128)(2,1)}, u32[]{:S(2)}) copy-start(bf16[1,1,32,128,128]{4,3,2,1,0:T(8,128)(2,1)} %param.4) | copy-start | bytes 3145732
  26.6 15.2 %copy-start.3 = (f32[64,1024]{1,0:T(8,128)S(1)}, f32[64,1024]{1,0:T(8,128)}, u32[]{:S(2)}) copy-start(f32[64,1024]{1,0:T(8,128)} %start_ref.1) | copy-start | bytes 786436
  26.6 4.5 %collective-permute-start.7 = (bf16[4,9,64,128]{3,2,1,0:T(8,128)(2,1)S(1)}, bf16[4,9,64,128]{3,2,1,0:T(8,128)(2,1)S(1)}, u32[]{:S(2)}, u32[]{:S(2)}) collective-permute-start(bf16[4,9,64,128]{3,2,1,0:T(8,128)(2,1)S(1)} %get-tuple-element.29), channel_id=1, source_target_pairs={{0,1},{1,0},{2,3},{3,2},{4,5},{5,4},{6,7},{7,6},{8,9},{9,8},{10,11... | collective-permute-start | bytes 1769480 | tf_op jit(solution)/shard_map/ppermute | solution.py:37
  26.7 8.8 %collective-permute-start.11 = (bf16[9,64,128]{2,1,0:T(8,128)(2,1)S(1)}, bf16[9,64,128]{2,1,0:T(8,128)(2,1)S(1)}, u32[]{:S(2)}, u32[]{:S(2)}) collective-permute-start(bf16[9,64,128]{2,1,0:T(8,128)(2,1)S(1)} %get-tuple-element.35), channel_id=1, source_target_pairs={{0,8},{8,0},{16,24},{24,16},{1,9},{9,1},{17,25},{25,17},{2,10},{10... | collective-permute-start | bytes 442376 | tf_op jit(solution)/shard_map/ppermute | solution.py:37
  26.8 14.0 %collective-permute-start.12 = (bf16[9,64,128]{2,1,0:T(8,128)(2,1)S(1)}, bf16[9,64,128]{2,1,0:T(8,128)(2,1)S(1)}, u32[]{:S(2)}, u32[]{:S(2)}) collective-permute-start(bf16[9,64,128]{2,1,0:T(8,128)(2,1)S(1)} %get-tuple-element.36), channel_id=1, source_target_pairs={{0,16},{8,24},{16,0},{24,8},{1,17},{9,25},{17,1},{25,9},{2,18},{10... | collective-permute-start | bytes 442376 | tf_op jit(solution)/shard_map/ppermute | solution.py:37
  29.2 11.5 %collective-permute-start.13 = (bf16[9,64,128]{2,1,0:T(8,128)(2,1)S(1)}, bf16[9,64,128]{2,1,0:T(8,128)(2,1)S(1)}, u32[]{:S(2)}, u32[]{:S(2)}) collective-permute-start(bf16[9,64,128]{2,1,0:T(8,128)(2,1)S(1)} %get-tuple-element.37), channel_id=1, source_target_pairs={{0,24},{8,16},{16,8},{24,0},{1,25},{9,17},{17,9},{25,1},{2,26},{10... | collective-permute-start | bytes 442376 | tf_op jit(solution)/shard_map/ppermute | solution.py:37
  31.3 29.6 %copy-start.1 = (bf16[1,1,32,128,128]{4,3,2,1,0:T(8,128)(2,1)S(1)}, bf16[1,1,32,128,128]{4,3,2,1,0:T(8,128)(2,1)}, u32[]{:S(2)}) copy-start(bf16[1,1,32,128,128]{4,3,2,1,0:T(8,128)(2,1)} %param.4) | copy-start | bytes 3145732
  31.3 29.6 %copy-start.5 = (s32[1,1,32]{2,1,0:T(1,128)S(1)}, s32[1,1,32]{2,1,0:T(1,128)}, u32[]{:S(2)}) copy-start(s32[1,1,32]{2,1,0:T(1,128)} %param.5) | copy-start | bytes 388
  31.3 29.6 %copy-start.7 = (s32[1,1,32]{2,1,0:T(1,128)S(1)}, s32[1,1,32]{2,1,0:T(1,128)}, u32[]{:S(2)}) copy-start(s32[1,1,32]{2,1,0:T(1,128)} %param.6) | copy-start | bytes 388
  31.3 9.5 %collective-permute-start.8 = (bf16[9,64,128]{2,1,0:T(8,128)(2,1)S(1)}, bf16[9,64,128]{2,1,0:T(8,128)(2,1)S(1)}, u32[]{:S(2)}, u32[]{:S(2)}) collective-permute-start(bf16[9,64,128]{2,1,0:T(8,128)(2,1)S(1)} %get-tuple-element.32), channel_id=1, source_target_pairs={{0,2},{1,3},{2,0},{3,1},{4,6},{5,7},{6,4},{7,5},{8,10},{9,11},{10,... | collective-permute-start | bytes 442376 | tf_op jit(solution)/shard_map/ppermute | solution.py:37
  32.9 7.9 %collective-permute-start.9 = (bf16[9,64,128]{2,1,0:T(8,128)(2,1)S(1)}, bf16[9,64,128]{2,1,0:T(8,128)(2,1)S(1)}, u32[]{:S(2)}, u32[]{:S(2)}) collective-permute-start(bf16[9,64,128]{2,1,0:T(8,128)(2,1)S(1)} %get-tuple-element.33), channel_id=1, source_target_pairs={{0,4},{1,5},{2,6},{3,7},{4,0},{5,1},{6,2},{7,3},{8,12},{9,13},{10,... | collective-permute-start | bytes 442376 | tf_op jit(solution)/shard_map/ppermute | solution.py:37
  35.5 6.3 %collective-permute-start.10 = (bf16[9,64,128]{2,1,0:T(8,128)(2,1)S(1)}, bf16[9,64,128]{2,1,0:T(8,128)(2,1)S(1)}, u32[]{:S(2)}, u32[]{:S(2)}) collective-permute-start(bf16[9,64,128]{2,1,0:T(8,128)(2,1)S(1)} %get-tuple-element.34), channel_id=1, source_target_pairs={{0,6},{1,7},{2,4},{3,5},{4,2},{5,3},{6,0},{7,1},{8,14},{9,15},{10,... | collective-permute-start | bytes 442376 | tf_op jit(solution)/shard_map/ppermute | solution.py:37
  42.0 1.9 %collective-permute-start.17 = (bf16[8,64,128]{2,1,0:T(8,128)(2,1)S(1)}, bf16[8,64,128]{2,1,0:T(8,128)(2,1)S(1)}, u32[]{:S(2)}, u32[]{:S(2)}) collective-permute-start(bf16[8,64,128]{2,1,0:T(8,128)(2,1)S(1)} %get-tuple-element.40.refs_0_), channel_id=1, source_target_pairs={{0,1},{1,0},{2,3},{3,2},{4,5},{5,4},{6,7},{7,6},{8,9},{9,8},{10,11... | collective-permute-start | bytes 393224 | tf_op jit(solution)/shard_map/ppermute | solution.py:37
  42.1 7.8 %collective-permute-start.16 = (bf16[8,64,128]{2,1,0:T(8,128)(2,1)S(1)}, bf16[8,64,128]{2,1,0:T(8,128)(2,1)S(1)}, u32[]{:S(2)}, u32[]{:S(2)}) collective-permute-start(bf16[8,64,128]{2,1,0:T(8,128)(2,1)S(1)} %get-tuple-element.40.refs_0_), channel_id=1, source_target_pairs={{0,24},{8,16},{16,8},{24,0},{1,25},{9,17},{17,9},{25,1},{2,26},{10... | collective-permute-start | bytes 393224 | tf_op jit(solution)/shard_map/ppermute | solution.py:37
  43.9 16.9 %collective-permute-start.20 = (bf16[2,8,64,128]{3,2,1,0:T(8,128)(2,1)S(1)}, bf16[2,8,64,128]{3,2,1,0:T(8,128)(2,1)S(1)}, u32[]{:S(2)}, u32[]{:S(2)}) collective-permute-start(bf16[2,8,64,128]{3,2,1,0:T(8,128)(2,1)S(1)} %pad_maximum_fusion.1.refs_4_), channel_id=1, source_target_pairs={{0,6},{1,7},{2,4},{3,5},{4,2},{5,3},{6,0},{7,1},{8,14},{9,15},{10,... | collective-permute-start | bytes 786440 | tf_op jit(solution)/shard_map/ppermute | solution.py:37
  46.0 14.9 %collective-permute-start.19 = (bf16[2,8,64,128]{3,2,1,0:T(8,128)(2,1)S(1)}, bf16[2,8,64,128]{3,2,1,0:T(8,128)(2,1)S(1)}, u32[]{:S(2)}, u32[]{:S(2)}) collective-permute-start(bf16[2,8,64,128]{3,2,1,0:T(8,128)(2,1)S(1)} %pad_maximum_fusion.1.refs_4_), channel_id=1, source_target_pairs={{0,4},{1,5},{2,6},{3,7},{4,0},{5,1},{6,2},{7,3},{8,12},{9,13},{10,... | collective-permute-start | bytes 786440 | tf_op jit(solution)/shard_map/ppermute | solution.py:37
  47.0 13.9 %collective-permute-start.18 = (bf16[2,8,64,128]{3,2,1,0:T(8,128)(2,1)S(1)}, bf16[2,8,64,128]{3,2,1,0:T(8,128)(2,1)S(1)}, u32[]{:S(2)}, u32[]{:S(2)}) collective-permute-start(bf16[2,8,64,128]{3,2,1,0:T(8,128)(2,1)S(1)} %pad_maximum_fusion.1.refs_4_), channel_id=1, source_target_pairs={{0,2},{1,3},{2,0},{3,1},{4,6},{5,7},{6,4},{7,5},{8,10},{9,11},{10,... | collective-permute-start | bytes 786440 | tf_op jit(solution)/shard_map/ppermute | solution.py:37
  47.5 10.6 %collective-permute-start.15 = (bf16[8,64,128]{2,1,0:T(8,128)(2,1)S(1)}, bf16[8,64,128]{2,1,0:T(8,128)(2,1)S(1)}, u32[]{:S(2)}, u32[]{:S(2)}) collective-permute-start(bf16[8,64,128]{2,1,0:T(8,128)(2,1)S(1)} %get-tuple-element.40.refs_0_), channel_id=1, source_target_pairs={{0,16},{8,24},{16,0},{24,8},{1,17},{9,25},{17,1},{25,9},{2,18},{10... | collective-permute-start | bytes 393224 | tf_op jit(solution)/shard_map/ppermute | solution.py:37
  49.9 10.9 %collective-permute-start.14 = (bf16[8,64,128]{2,1,0:T(8,128)(2,1)S(1)}, bf16[8,64,128]{2,1,0:T(8,128)(2,1)S(1)}, u32[]{:S(2)}, u32[]{:S(2)}) collective-permute-start(bf16[8,64,128]{2,1,0:T(8,128)(2,1)S(1)} %get-tuple-element.40.refs_0_), channel_id=1, source_target_pairs={{0,8},{8,0},{16,24},{24,16},{1,9},{9,1},{17,25},{25,17},{2,10},{10... | collective-permute-start | bytes 393224 | tf_op jit(solution)/shard_map/ppermute | solution.py:37
  62.7 4.5 %collective-permute-start.21 = (bf16[4,8,64,128]{3,2,1,0:T(8,128)(2,1)S(1)}, bf16[4,8,64,128]{3,2,1,0:T(8,128)(2,1)S(1)}, u32[]{:S(2)}, u32[]{:S(2)}) collective-permute-start(bf16[4,8,64,128]{3,2,1,0:T(8,128)(2,1)S(1)} %get-tuple-element.42), channel_id=1, source_target_pairs={{0,1},{1,0},{2,3},{3,2},{4,5},{5,4},{6,7},{7,6},{8,9},{9,8},{10,11... | collective-permute-start | bytes 1572872 | tf_op jit(solution)/shard_map/ppermute | solution.py:37
  62.8 8.1 %collective-permute-start.25 = (bf16[8,64,128]{2,1,0:T(8,128)(2,1)S(1)}, bf16[8,64,128]{2,1,0:T(8,128)(2,1)S(1)}, u32[]{:S(2)}, u32[]{:S(2)}) collective-permute-start(bf16[8,64,128]{2,1,0:T(8,128)(2,1)S(1)} %get-tuple-element.48), channel_id=1, source_target_pairs={{0,8},{8,0},{16,24},{24,16},{1,9},{9,1},{17,25},{25,17},{2,10},{10... | collective-permute-start | bytes 393224 | tf_op jit(solution)/shard_map/ppermute | solution.py:37
  63.1 12.9 %collective-permute-start.26 = (bf16[8,64,128]{2,1,0:T(8,128)(2,1)S(1)}, bf16[8,64,128]{2,1,0:T(8,128)(2,1)S(1)}, u32[]{:S(2)}, u32[]{:S(2)}) collective-permute-start(bf16[8,64,128]{2,1,0:T(8,128)(2,1)S(1)} %get-tuple-element.49), channel_id=1, source_target_pairs={{0,16},{8,24},{16,0},{24,8},{1,17},{9,25},{17,1},{25,9},{2,18},{10... | collective-permute-start | bytes 393224 | tf_op jit(solution)/shard_map/ppermute | solution.py:37
  65.4 10.6 %collective-permute-start.27 = (bf16[8,64,128]{2,1,0:T(8,128)(2,1)S(1)}, bf16[8,64,128]{2,1,0:T(8,128)(2,1)S(1)}, u32[]{:S(2)}, u32[]{:S(2)}) collective-permute-start(bf16[8,64,128]{2,1,0:T(8,128)(2,1)S(1)} %get-tuple-element.50), channel_id=1, source_target_pairs={{0,24},{8,16},{16,8},{24,0},{1,25},{9,17},{17,9},{25,1},{2,26},{10... | collective-permute-start | bytes 393224 | tf_op jit(solution)/shard_map/ppermute | solution.py:37
  67.4 8.7 %collective-permute-start.22 = (bf16[8,64,128]{2,1,0:T(8,128)(2,1)S(1)}, bf16[8,64,128]{2,1,0:T(8,128)(2,1)S(1)}, u32[]{:S(2)}, u32[]{:S(2)}) collective-permute-start(bf16[8,64,128]{2,1,0:T(8,128)(2,1)S(1)} %get-tuple-element.45), channel_id=1, source_target_pairs={{0,2},{1,3},{2,0},{3,1},{4,6},{5,7},{6,4},{7,5},{8,10},{9,11},{10,... | collective-permute-start | bytes 393224 | tf_op jit(solution)/shard_map/ppermute | solution.py:37
  69.0 7.1 %collective-permute-start.23 = (bf16[8,64,128]{2,1,0:T(8,128)(2,1)S(1)}, bf16[8,64,128]{2,1,0:T(8,128)(2,1)S(1)}, u32[]{:S(2)}, u32[]{:S(2)}) collective-permute-start(bf16[8,64,128]{2,1,0:T(8,128)(2,1)S(1)} %get-tuple-element.46), channel_id=1, source_target_pairs={{0,4},{1,5},{2,6},{3,7},{4,0},{5,1},{6,2},{7,3},{8,12},{9,13},{10,... | collective-permute-start | bytes 393224 | tf_op jit(solution)/shard_map/ppermute | solution.py:37
  70.9 6.0 %collective-permute-start.24 = (bf16[8,64,128]{2,1,0:T(8,128)(2,1)S(1)}, bf16[8,64,128]{2,1,0:T(8,128)(2,1)S(1)}, u32[]{:S(2)}, u32[]{:S(2)}) collective-permute-start(bf16[8,64,128]{2,1,0:T(8,128)(2,1)S(1)} %get-tuple-element.47), channel_id=1, source_target_pairs={{0,6},{1,7},{2,4},{3,5},{4,2},{5,3},{6,0},{7,1},{8,14},{9,15},{10,... | collective-permute-start | bytes 393224 | tf_op jit(solution)/shard_map/ppermute | solution.py:37
  77.7 2.0 %collective-permute-start.31 = (bf16[8,64,128]{2,1,0:T(8,128)(2,1)S(1)}, bf16[8,64,128]{2,1,0:T(8,128)(2,1)S(1)}, u32[]{:S(2)}, u32[]{:S(2)}) collective-permute-start(bf16[8,64,128]{2,1,0:T(8,128)(2,1)S(1)} %get-tuple-element.53.refs_0_), channel_id=1, source_target_pairs={{0,1},{1,0},{2,3},{3,2},{4,5},{5,4},{6,7},{7,6},{8,9},{9,8},{10,11... | collective-permute-start | bytes 393224 | tf_op jit(solution)/shard_map/ppermute | solution.py:37
  77.7 7.8 %collective-permute-start.30 = (bf16[8,64,128]{2,1,0:T(8,128)(2,1)S(1)}, bf16[8,64,128]{2,1,0:T(8,128)(2,1)S(1)}, u32[]{:S(2)}, u32[]{:S(2)}) collective-permute-start(bf16[8,64,128]{2,1,0:T(8,128)(2,1)S(1)} %get-tuple-element.53.refs_0_), channel_id=1, source_target_pairs={{0,24},{8,16},{16,8},{24,0},{1,25},{9,17},{17,9},{25,1},{2,26},{10... | collective-permute-start | bytes 393224 | tf_op jit(solution)/shard_map/ppermute | solution.py:37
  79.6 16.5 %collective-permute-start.34 = (bf16[2,8,64,128]{3,2,1,0:T(8,128)(2,1)S(1)}, bf16[2,8,64,128]{3,2,1,0:T(8,128)(2,1)S(1)}, u32[]{:S(2)}, u32[]{:S(2)}) collective-permute-start(bf16[2,8,64,128]{3,2,1,0:T(8,128)(2,1)S(1)} %pad_maximum_fusion.2.refs_4_), channel_id=1, source_target_pairs={{0,6},{1,7},{2,4},{3,5},{4,2},{5,3},{6,0},{7,1},{8,14},{9,15},{10,... | collective-permute-start | bytes 786440 | tf_op jit(solution)/shard_map/ppermute | solution.py:37
  81.6 14.5 %collective-permute-start.33 = (bf16[2,8,64,128]{3,2,1,0:T(8,128)(2,1)S(1)}, bf16[2,8,64,128]{3,2,1,0:T(8,128)(2,1)S(1)}, u32[]{:S(2)}, u32[]{:S(2)}) collective-permute-start(bf16[2,8,64,128]{3,2,1,0:T(8,128)(2,1)S(1)} %pad_maximum_fusion.2.refs_4_), channel_id=1, source_target_pairs={{0,4},{1,5},{2,6},{3,7},{4,0},{5,1},{6,2},{7,3},{8,12},{9,13},{10,... | collective-permute-start | bytes 786440 | tf_op jit(solution)/shard_map/ppermute | solution.py:37
  82.6 13.5 %collective-permute-start.32 = (bf16[2,8,64,128]{3,2,1,0:T(8,128)(2,1)S(1)}, bf16[2,8,64,128]{3,2,1,0:T(8,128)(2,1)S(1)}, u32[]{:S(2)}, u32[]{:S(2)}) collective-permute-start(bf16[2,8,64,128]{3,2,1,0:T(8,128)(2,1)S(1)} %pad_maximum_fusion.2.refs_4_), channel_id=1, source_target_pairs={{0,2},{1,3},{2,0},{3,1},{4,6},{5,7},{6,4},{7,5},{8,10},{9,11},{10,... | collective-permute-start | bytes 786440 | tf_op jit(solution)/shard_map/ppermute | solution.py:37
  83.2 10.2 %collective-permute-start.29 = (bf16[8,64,128]{2,1,0:T(8,128)(2,1)S(1)}, bf16[8,64,128]{2,1,0:T(8,128)(2,1)S(1)}, u32[]{:S(2)}, u32[]{:S(2)}) collective-permute-start(bf16[8,64,128]{2,1,0:T(8,128)(2,1)S(1)} %get-tuple-element.53.refs_0_), channel_id=1, source_target_pairs={{0,16},{8,24},{16,0},{24,8},{1,17},{9,25},{17,1},{25,9},{2,18},{10... | collective-permute-start | bytes 393224 | tf_op jit(solution)/shard_map/ppermute | solution.py:37
  85.6 10.5 %collective-permute-start.28 = (bf16[8,64,128]{2,1,0:T(8,128)(2,1)S(1)}, bf16[8,64,128]{2,1,0:T(8,128)(2,1)S(1)}, u32[]{:S(2)}, u32[]{:S(2)}) collective-permute-start(bf16[8,64,128]{2,1,0:T(8,128)(2,1)S(1)} %get-tuple-element.53.refs_0_), channel_id=1, source_target_pairs={{0,8},{8,0},{16,24},{24,16},{1,9},{9,1},{17,25},{25,17},{2,10},{10... | collective-permute-start | bytes 393224 | tf_op jit(solution)/shard_map/ppermute | solution.py:37
  98.4 1.2 %collective-permute-start.35 = (f32[40,128]{1,0:T(8,128)S(1)}, f32[40,128]{1,0:T(8,128)S(1)}, u32[]{:S(2)}, u32[]{:S(2)}) collective-permute-start(f32[40,128]{1,0:T(8,128)S(1)} %shard_map.66), channel_id=1, source_target_pairs={{0,1},{1,0},{2,3},{3,2},{4,5},{5,4},{6,7},{7,6},{8,9},{9,8},{10,11... | collective-permute-start | bytes 61448 | tf_op jit(solution)/shard_map/ppermute | solution.py:37
  99.6 4.7 %collective-permute-start.38 = (f32[40,128]{1,0:T(8,128)S(1)}, f32[40,128]{1,0:T(8,128)S(1)}, u32[]{:S(2)}, u32[]{:S(2)}) collective-permute-start(f32[40,128]{1,0:T(8,128)S(1)} %add.12), channel_id=1, source_target_pairs={{0,6},{1,7},{2,4},{3,5},{4,2},{5,3},{6,0},{7,1},{8,14},{9,15},{10,... | collective-permute-start | bytes 61448 | tf_op jit(solution)/shard_map/ppermute | solution.py:37
  101.6 3.8 %collective-permute-start.37 = (f32[40,128]{1,0:T(8,128)S(1)}, f32[40,128]{1,0:T(8,128)S(1)}, u32[]{:S(2)}, u32[]{:S(2)}) collective-permute-start(f32[40,128]{1,0:T(8,128)S(1)} %add.12), channel_id=1, source_target_pairs={{0,4},{1,5},{2,6},{3,7},{4,0},{5,1},{6,2},{7,3},{8,12},{9,13},{10,... | collective-permute-start | bytes 61448 | tf_op jit(solution)/shard_map/ppermute | solution.py:37
  102.6 3.8 %collective-permute-start.36 = (f32[40,128]{1,0:T(8,128)S(1)}, f32[40,128]{1,0:T(8,128)S(1)}, u32[]{:S(2)}, u32[]{:S(2)}) collective-permute-start(f32[40,128]{1,0:T(8,128)S(1)} %add.12), channel_id=1, source_target_pairs={{0,2},{1,3},{2,0},{3,1},{4,6},{5,7},{6,4},{7,5},{8,10},{9,11},{10,... | collective-permute-start | bytes 61448 | tf_op jit(solution)/shard_map/ppermute | solution.py:37
  106.4 5.6 %collective-permute-start.41 = (f32[40,128]{1,0:T(8,128)S(1)}, f32[40,128]{1,0:T(8,128)S(1)}, u32[]{:S(2)}, u32[]{:S(2)}) collective-permute-start(f32[40,128]{1,0:T(8,128)S(1)} %add_add_fusion.refs_0_), channel_id=1, source_target_pairs={{0,24},{8,16},{16,8},{24,0},{1,25},{9,17},{17,9},{25,1},{2,26},{10... | collective-permute-start | bytes 61448 | tf_op jit(solution)/shard_map/ppermute | solution.py:37
  108.5 4.7 %collective-permute-start.40 = (f32[40,128]{1,0:T(8,128)S(1)}, f32[40,128]{1,0:T(8,128)S(1)}, u32[]{:S(2)}, u32[]{:S(2)}) collective-permute-start(f32[40,128]{1,0:T(8,128)S(1)} %add_add_fusion.refs_0_), channel_id=1, source_target_pairs={{0,16},{8,24},{16,0},{24,8},{1,17},{9,25},{17,1},{25,9},{2,18},{10... | collective-permute-start | bytes 61448 | tf_op jit(solution)/shard_map/ppermute | solution.py:37
  108.5 4.7 %collective-permute-start.39 = (f32[40,128]{1,0:T(8,128)S(1)}, f32[40,128]{1,0:T(8,128)S(1)}, u32[]{:S(2)}, u32[]{:S(2)}) collective-permute-start(f32[40,128]{1,0:T(8,128)S(1)} %add_add_fusion.refs_0_), channel_id=1, source_target_pairs={{0,8},{8,0},{16,24},{24,16},{1,9},{9,1},{17,25},{25,17},{2,10},{10... | collective-permute-start | bytes 61448 | tf_op jit(solution)/shard_map/ppermute | solution.py:37
  (2 other events, 1.3 us)

commit v6 on v5

--- a/solution.py
+++ b/solution.py
@@ -70,13 +70,11 @@
     )
 
 
-def fill(panel, part_refs):
-    place_at = 0
-    for part in part_refs:
-        blocks = part.reshape(-1, *part.shape[-2:])
-        count = blocks.shape[0]
-        panel[place_at : place_at + count, : part.shape[-2], :] = blocks[...]
-        place_at += count
+def fill(panel, parts, offsets):
+    blocks = [part.at[d] for part in parts for d in range(part.shape[0])]
+    for block, offset in zip(blocks, offsets):
+        group, height, _ = block.shape
+        panel[offset * group : (offset + 1) * group, :height, :] = block[...]
 
 
 def place(tile, group, me, halves):
@@ -86,15 +84,17 @@
     return apart * group + tile % group
 
 
-def product_kernel(counts, degree, meta, tile_rows, tile_cols, tiles_ref, *refs):
-    cols_n, rows_n, half = counts
-    col_parts, refs = refs[:cols_n], refs[cols_n:]
-    row_parts, refs = refs[:rows_n], refs[rows_n:]
+def product_kernel(offsets, degree, meta, tile_rows, tile_cols, tiles_ref, *refs):
+    col_offsets, row_offsets = offsets
+    half = len(row_offsets) // 2
+    row_end = 2 + len(row_offsets)
+    col_parts, row_parts, refs = refs[:2], refs[2:row_end], refs[row_end:]
     kept_ref, swap_ref, own_ref, *send_refs = refs[:-4]
     col_panel, row_panel, row_total, col_total = refs[-4:]
-    group, vectors_n, width = col_parts[0].shape
-    for panel, parts in ((col_panel, col_parts), (row_panel, row_parts)):
-        fill(panel, parts)
+    group, vectors_n, width = col_parts[0].shape[1:]
+    panels = ((col_panel, col_parts, col_offsets), (row_panel, row_parts, row_offsets))
+    for panel, parts, places in panels:
+        fill(panel, parts, places)
         if degree:
             panel[:, vectors_n:, :] = jnp.ones(
                 (panel.shape[0], panel.shape[1] - vectors_n, width), BF16
@@ -122,9 +122,9 @@
             send[group] = split_degree(degree_of(total, d * group, group, vectors_n), vectors_n)
 
 
-def products(tiles, tile_rows, tile_cols, meta, col_parts, row_parts, degree):
-    group, vectors_n, width = col_parts[0].shape
-    rows_n, half = len(col_parts), len(row_parts)
+def products(tiles, tile_rows, tile_cols, meta, col_parts, row_parts, offsets, degree):
+    group, vectors_n, width = col_parts[0].shape[1:]
+    rows_n, half = len(offsets[0]), len(offsets[1]) // 2
     height = vectors_n + (DEGREE_ROWS if degree else 0)
     blocks = group + (1 if degree else 0)
     out_shape = [
@@ -139,7 +139,7 @@
         pltpu.VMEM((2 * half * group, height, width), F32),
         pltpu.VMEM((rows_n * group, height, width), F32),
     ]
-    kernel = functools.partial(product_kernel, (rows_n, half, half), degree)
+    kernel = functools.partial(product_kernel, offsets, degree)
     args = [meta, tile_rows, tile_cols, tiles, *col_parts, *row_parts]
     kept, swap, own, *send = call(kernel, out_shape, scratch, 32, args, 4 * tiles.size * height, 3)
     return kept, swap, own, send
@@ -224,13 +224,13 @@
     )
 
 
-def form_kernel(counts, meta, tile_rows, tile_cols, tiles_ref, gram_ref, *refs):
-    cols_n, rows_n = counts
-    col_parts, refs = refs[:cols_n], refs[cols_n:]
-    row_parts, (out_ref, col_panel, row_panel, left, right) = refs[:rows_n], refs[rows_n:]
-    group, vectors_n, width = col_parts[0].shape
-    fill(col_panel, col_parts)
-    fill(row_panel, row_parts)
+def form_kernel(offsets, meta, tile_rows, tile_cols, tiles_ref, gram_ref, *refs):
+    row_end = 2 + len(offsets[1])
+    col_parts, row_parts, refs = refs[:2], refs[2:row_end], refs[row_end:]
+    out_ref, col_panel, row_panel, left, right = refs
+    group, vectors_n, width = col_parts[0].shape[1:]
+    fill(col_panel, col_parts, offsets[0])
+    fill(row_panel, row_parts, offsets[1])
     for t in range(tiles_ref.shape[0]):
         columns = slice(t * width, (t + 1) * width)
         left[:, columns] = row_panel[place(tile_rows[t], group, meta[1], 0)]
@@ -321,14 +321,27 @@
     chips_n = cols_n // 2
 
     def gather(rounded):
-        col_parts = [rounded, *exchange([rounded] * (rows_n - 1), "row")]
-        pair = jnp.stack([rounded, trade(rounded, "col", 1)])
-        return col_parts, [pair, *exchange([pair] * (chips_n - 1), "col", 2)]
+        held, d = rounded[None], rows_n // 2
+        while d:
+            got = trade(held, "row", d)
+            if d > 1:
+                held = jnp.concatenate([held, got])
+            d //= 2
+        chips = [rounded, *exchange([rounded] * (chips_n - 1), "col", 2)]
+        chips += [trade(chip, "col", 1) for chip in chips]
+        return [held, got], [chip[None] for chip in chips]
+
+    col_offsets, d = [0], rows_n // 2
+    while d:
+        col_offsets += [offset ^ d for offset in col_offsets]
+        d //= 2
+    row_offsets = [2 * d + core for core in range(2) for d in range(chips_n)]
+    offsets = (col_offsets, row_offsets)
 
     def apply(rounded, degree):
         col_parts, row_parts = gather(rounded)
         kept, send, col_own, col_send = products(
-            tiles, tile_rows, tile_cols, meta, col_parts, row_parts, degree
+            tiles, tile_rows, tile_cols, meta, col_parts, row_parts, offsets, degree
         )
         col_got = exchange(col_send, "row")
         row_own, row_send = merge(kept, trade(send, "col", 1), degree)
@@ -355,7 +368,7 @@
     col_parts, row_parts = gather(rounded)
     spread = (vectors_n, tiles.shape[0] * width)
     sums = call(
-        functools.partial(form_kernel, (len(col_parts), len(row_parts))),
+        functools.partial(form_kernel, offsets),
         jax.ShapeDtypeStruct((vectors_n // 2 + 8, 2 * vectors_n), F32),
         [
             pltpu.VMEM((rows_n * group, vectors_n, width), BF16),

time: 121 us -> 113 us (0.934)
  starting transfers between devices: 67.5 us -> 52.5 us
  waiting for transfers between devices: 33.7 us -> 41.3 us
    ppermute x42 -> x48, starting transfers between devices: 67.5 us -> 52.5 us  [trade(): return lax.ppermute(part, axis, [(i, i ^ d) for i in range(n)])]
    ppermute x42 -> x48, waiting for transfers between devices: 33.7 us -> 41.3 us  [trade(): return lax.ppermute(part, axis, [(i, i ^ d) for i in range(n)])]
  transfers between devices with their start and end apart: 42 -> 48, of which waited for: 23 -> 30; matrix products, arithmetic and copies ran while one was open for 0% -> 0% of each run, Pallas kernels for 0% -> 0%
where the time goes in v6:
time: 113 us
  starting transfers between devices  52.5 us (46%)
  waiting for transfers between devices  41.3 us (37%)
  Pallas kernels  14.7 us (13%)
  local copies, waits for them, and re-layouts  3.5 us (3%)
    ppermute x48, starting transfers between devices, trade(): return lax.ppermute(part, axis, [(i, i ^ d) for i in range(n)])  52.5 us
    ppermute x48, waiting for transfers between devices, trade(): return lax.ppermute(part, axis, [(i, i ^ d) for i in range(n)])  41.3 us
    pallas_call x9, Pallas kernels, call(): pl.pallas_call(kernel, out_shape=out_shape, in_specs=[SMEM] * smem + [VME...  14.7 us
    unnamed x16, local copies, waits for them, and re-layouts  3.5 us
  transfers between devices with their start and end apart: 48, of which 30 were waited for; matrix products, arithmetic and copies ran while one was open for 0% of the time, Pallas kernels for 0%

profile of v6, /device:TPU:0, one launch (start us, length us, event | category | flops | bytes accessed | tf_op | source)
XLA Modules:
  0.0 113.0 jit_solution(6630795076624000228)
XLA Ops:
  0.6 0.9 copy-done.2
  1.6 4.1 %collective-permute-start = (bf16[1,8,64,128]{3,2,1,0:T(8,128)(2,1)S(1)}, bf16[1,8,64,128]{3,2,1,0:T(8,128)(2,1)S(1)}, u32[]{:S(2)}, u32[]{:S(2)}) collective-permute-start(bf16[1,8,64,128]{3,2,1,0:T(8,128)(2,1)S(1)} %bitcast.32), channel_id=1, source_target_pairs={{0,16},{8,24},{16,0},{24,8},{1,17},{9,25},{17,1},{25,9},{2,18},{10... | collective-permute-start | bytes 393224 | tf_op jit(solution)/shard_map/ppermute | solution.py:37
  5.7 2.4 %collective-permute-start.4 = (bf16[8,64,128]{2,1,0:T(8,128)(2,1)S(1)}, bf16[8,64,128]{2,1,0:T(8,128)(2,1)S(1)}, u32[]{:S(2)}, u32[]{:S(2)}) collective-permute-start(bf16[8,64,128]{2,1,0:T(8,128)(2,1)S(1)} %shard_map.59), channel_id=1, source_target_pairs={{0,6},{1,7},{2,4},{3,5},{4,2},{5,3},{6,0},{7,1},{8,14},{9,15},{10,... | collective-permute-start | bytes 393224 | tf_op jit(solution)/shard_map/ppermute | solution.py:37
  9.2 2.8 %collective-permute-done = bf16[1,8,64,128]{3,2,1,0:T(8,128)(2,1)S(1)} collective-permute-done((bf16[1,8,64,128]{3,2,1,0:T(8,128)(2,1)S(1)}, bf16[1,8,64,128]{3,2,1,0:T(8,128)(2,1)S(1)}, u32[]{:S(2)}, u32[]{:S(2)}) %collective-permute-start) | collective-permute-done | bytes 131104 | tf_op jit(solution)/shard_map/ppermute | solution.py:37
  12.0 0.8 collective-permute-start.1
  13.3 1.0 collective-permute-done.3
  15.0 0.8 collective-permute-done.7
  15.9 3.7 %collective-permute-done.1.refs_1_ = bf16[2,8,64,128]{3,2,1,0:T(8,128)(2,1)S(1)} collective-permute-done((bf16[2,8,64,128]{3,2,1,0:T(8,128)(2,1)S(1)}, bf16[2,8,64,128]{3,2,1,0:T(8,128)(2,1)S(1)}, u32[]{:S(2)}, u32[]{:S(2)}) %collective-permute-start.1) | collective-permute-done | bytes 262176 | tf_op jit(solution)/shard_map/ppermute | solution.py:37
  19.6 1.2 %copy-done = bf16[1,1,32,128,128]{4,3,2,1,0:T(8,128)(2,1)S(1)} copy-done((bf16[1,1,32,128,128]{4,3,2,1,0:T(8,128)(2,1)S(1)}, bf16[1,1,32,128,128]{4,3,2,1,0:T(8,128)(2,1)}, u32[]{:S(2)}) %copy-start) | copy-done | bytes 1048600
  22.1 2.2 %shard_map.60 = (f32[4,8,80,128]{3,2,1,0:T(8,128)S(1)}, bf16[4,9,64,128]{3,2,1,0:T(8,128)(2,1)S(1)}, f32[8,80,128]{2,1,0:T(8,128)S(1)}, bf16[9,64,128]{2,1,0:T(8...) custom-call(s32[2]{0:T(128)S(1)} %pad_add_fusion.meta, s32[32]{0:T(128)S(1)} %bitcast.62, ...), custom_call_target="tpu_custom_call" | custom-call | flops 167772160 | bytes 2621704 | tf_op jit(solution)/shard_map/pallas_call | solution.py:24
  24.4 1.5 %collective-permute-start.13 = (bf16[9,64,128]{2,1,0:T(8,128)(2,1)S(1)}, bf16[9,64,128]{2,1,0:T(8,128)(2,1)S(1)}, u32[]{:S(2)}, u32[]{:S(2)}) collective-permute-start(bf16[9,64,128]{2,1,0:T(8,128)(2,1)S(1)} %get-tuple-element.35), channel_id=1, source_target_pairs={{0,8},{8,0},{16,24},{24,16},{1,9},{9,1},{17,25},{25,17},{2,10},{10... | collective-permute-start | bytes 442376 | tf_op jit(solution)/shard_map/ppermute | solution.py:37
  25.9 3.4 %collective-permute-start.14 = (bf16[9,64,128]{2,1,0:T(8,128)(2,1)S(1)}, bf16[9,64,128]{2,1,0:T(8,128)(2,1)S(1)}, u32[]{:S(2)}, u32[]{:S(2)}) collective-permute-start(bf16[9,64,128]{2,1,0:T(8,128)(2,1)S(1)} %get-tuple-element.36), channel_id=1, source_target_pairs={{0,16},{8,24},{16,0},{24,8},{1,17},{9,25},{17,1},{25,9},{2,18},{10... | collective-permute-start | bytes 442376 | tf_op jit(solution)/shard_map/ppermute | solution.py:37
  29.5 1.6 %collective-permute-start.10 = (bf16[9,64,128]{2,1,0:T(8,128)(2,1)S(1)}, bf16[9,64,128]{2,1,0:T(8,128)(2,1)S(1)}, u32[]{:S(2)}, u32[]{:S(2)}) collective-permute-start(bf16[9,64,128]{2,1,0:T(8,128)(2,1)S(1)} %get-tuple-element.32), channel_id=1, source_target_pairs={{0,2},{1,3},{2,0},{3,1},{4,6},{5,7},{6,4},{7,5},{8,10},{9,11},{10,... | collective-permute-start | bytes 442376 | tf_op jit(solution)/shard_map/ppermute | solution.py:37
  31.0 1.5 %collective-permute-start.11 = (bf16[9,64,128]{2,1,0:T(8,128)(2,1)S(1)}, bf16[9,64,128]{2,1,0:T(8,128)(2,1)S(1)}, u32[]{:S(2)}, u32[]{:S(2)}) collective-permute-start(bf16[9,64,128]{2,1,0:T(8,128)(2,1)S(1)} %get-tuple-element.33), channel_id=1, source_target_pairs={{0,4},{1,5},{2,6},{3,7},{4,0},{5,1},{6,2},{7,3},{8,12},{9,13},{10,... | collective-permute-start | bytes 442376 | tf_op jit(solution)/shard_map/ppermute | solution.py:37
  32.5 0.8 collective-permute-done.13.refs_3_
  33.3 1.9 %collective-permute-start.12 = (bf16[9,64,128]{2,1,0:T(8,128)(2,1)S(1)}, bf16[9,64,128]{2,1,0:T(8,128)(2,1)S(1)}, u32[]{:S(2)}, u32[]{:S(2)}) collective-permute-start(bf16[9,64,128]{2,1,0:T(8,128)(2,1)S(1)} %get-tuple-element.34), channel_id=1, source_target_pairs={{0,6},{1,7},{2,4},{3,5},{4,2},{5,3},{6,0},{7,1},{8,14},{9,15},{10,... | collective-permute-start | bytes 442376 | tf_op jit(solution)/shard_map/ppermute | solution.py:37
  35.3 5.0 %collective-permute-done.14.refs_4_ = bf16[9,64,128]{2,1,0:T(8,128)(2,1)S(1)} collective-permute-done((bf16[9,64,128]{2,1,0:T(8,128)(2,1)S(1)}, bf16[9,64,128]{2,1,0:T(8,128)(2,1)S(1)}, u32[]{:S(2)}, u32[]{:S(2)}) %collective-permute-start.14) | collective-permute-done | bytes 147488 | tf_op jit(solution)/shard_map/ppermute | solution.py:37
  40.5 4.2 %collective-permute-start.16 = (bf16[1,8,64,128]{3,2,1,0:T(8,128)(2,1)S(1)}, bf16[1,8,64,128]{3,2,1,0:T(8,128)(2,1)S(1)}, u32[]{:S(2)}, u32[]{:S(2)}) collective-permute-start(bf16[1,8,64,128]{3,2,1,0:T(8,128)(2,1)S(1)} %bitcast.35), channel_id=1, source_target_pairs={{0,16},{8,24},{16,0},{24,8},{1,17},{9,25},{17,1},{25,9},{2,18},{10... | collective-permute-start | bytes 393224 | tf_op jit(solution)/shard_map/ppermute | solution.py:37
  44.8 2.5 %collective-permute-start.20 = (bf16[8,64,128]{2,1,0:T(8,128)(2,1)S(1)}, bf16[8,64,128]{2,1,0:T(8,128)(2,1)S(1)}, u32[]{:S(2)}, u32[]{:S(2)}) collective-permute-start(bf16[8,64,128]{2,1,0:T(8,128)(2,1)S(1)} %get-tuple-element.40), channel_id=1, source_target_pairs={{0,6},{1,7},{2,4},{3,5},{4,2},{5,3},{6,0},{7,1},{8,14},{9,15},{10,... | collective-permute-start | bytes 393224 | tf_op jit(solution)/shard_map/ppermute | solution.py:37
  48.2 2.4 %collective-permute-done.16 = bf16[1,8,64,128]{3,2,1,0:T(8,128)(2,1)S(1)} collective-permute-done((bf16[1,8,64,128]{3,2,1,0:T(8,128)(2,1)S(1)}, bf16[1,8,64,128]{3,2,1,0:T(8,128)(2,1)S(1)}, u32[]{:S(2)}, u32[]{:S(2)}) %collective-permute-start.16) | collective-permute-done | bytes 131104 | tf_op jit(solution)/shard_map/ppermute | solution.py:37
  51.5 1.4 %collective-permute-done.19 = bf16[8,64,128]{2,1,0:T(8,128)(2,1)S(1)} collective-permute-done((bf16[8,64,128]{2,1,0:T(8,128)(2,1)S(1)}, bf16[8,64,128]{2,1,0:T(8,128)(2,1)S(1)}, u32[]{:S(2)}, u32[]{:S(2)}) %collective-permute-start.19) | collective-permute-done | bytes 131104 | tf_op jit(solution)/shard_map/ppermute | solution.py:37
  53.4 0.8 collective-permute-done.23
  54.5 2.7 %collective-permute-done.17.refs_1_ = bf16[2,8,64,128]{3,2,1,0:T(8,128)(2,1)S(1)} collective-permute-done((bf16[2,8,64,128]{3,2,1,0:T(8,128)(2,1)S(1)}, bf16[2,8,64,128]{3,2,1,0:T(8,128)(2,1)S(1)}, u32[]{:S(2)}, u32[]{:S(2)}) %collective-permute-start.17) | collective-permute-done | bytes 262176 | tf_op jit(solution)/shard_map/ppermute | solution.py:37
  57.1 1.9 %shard_map.63 = (f32[4,8,64,128]{3,2,1,0:T(8,128)S(1)}, bf16[4,8,64,128]{3,2,1,0:T(8,128)(2,1)S(1)}, f32[8,64,128]{2,1,0:T(8,128)S(1)}, bf16[8,64,128]{2,1,0:T(8...) custom-call(s32[2]{0:T(128)S(1)} %pad_add_fusion.meta, s32[32]{0:T(128)S(1)} %bitcast.63, ...), custom_call_target="tpu_custom_call" | custom-call | flops 134217728 | bytes 2621704 | tf_op jit(solution)/shard_map/pallas_call | solution.py:24
  59.2 2.3 %collective-permute-start.30 = (bf16[8,64,128]{2,1,0:T(8,128)(2,1)S(1)}, bf16[8,64,128]{2,1,0:T(8,128)(2,1)S(1)}, u32[]{:S(2)}, u32[]{:S(2)}) collective-permute-start(bf16[8,64,128]{2,1,0:T(8,128)(2,1)S(1)} %get-tuple-element.49), channel_id=1, source_target_pairs={{0,16},{8,24},{16,0},{24,8},{1,17},{9,25},{17,1},{25,9},{2,18},{10... | collective-permute-start | bytes 393224 | tf_op jit(solution)/shard_map/ppermute | solution.py:37
  61.5 2.0 %collective-permute-start.31 = (bf16[8,64,128]{2,1,0:T(8,128)(2,1)S(1)}, bf16[8,64,128]{2,1,0:T(8,128)(2,1)S(1)}, u32[]{:S(2)}, u32[]{:S(2)}) collective-permute-start(bf16[8,64,128]{2,1,0:T(8,128)(2,1)S(1)} %get-tuple-element.50), channel_id=1, source_target_pairs={{0,24},{8,16},{16,8},{24,0},{1,25},{9,17},{17,9},{25,1},{2,26},{10... | collective-permute-start | bytes 393224 | tf_op jit(solution)/shard_map/ppermute | solution.py:37
  63.7 1.6 %collective-permute-start.26 = (bf16[8,64,128]{2,1,0:T(8,128)(2,1)S(1)}, bf16[8,64,128]{2,1,0:T(8,128)(2,1)S(1)}, u32[]{:S(2)}, u32[]{:S(2)}) collective-permute-start(bf16[8,64,128]{2,1,0:T(8,128)(2,1)S(1)} %get-tuple-element.45), channel_id=1, source_target_pairs={{0,2},{1,3},{2,0},{3,1},{4,6},{5,7},{6,4},{7,5},{8,10},{9,11},{10,... | collective-permute-start | bytes 393224 | tf_op jit(solution)/shard_map/ppermute | solution.py:37
  65.2 1.5 %collective-permute-start.27 = (bf16[8,64,128]{2,1,0:T(8,128)(2,1)S(1)}, bf16[8,64,128]{2,1,0:T(8,128)(2,1)S(1)}, u32[]{:S(2)}, u32[]{:S(2)}) collective-permute-start(bf16[8,64,128]{2,1,0:T(8,128)(2,1)S(1)} %get-tuple-element.46), channel_id=1, source_target_pairs={{0,4},{1,5},{2,6},{3,7},{4,0},{5,1},{6,2},{7,3},{8,12},{9,13},{10,... | collective-permute-start | bytes 393224 | tf_op jit(solution)/shard_map/ppermute | solution.py:37
  67.0 2.4 %collective-permute-start.28 = (bf16[8,64,128]{2,1,0:T(8,128)(2,1)S(1)}, bf16[8,64,128]{2,1,0:T(8,128)(2,1)S(1)}, u32[]{:S(2)}, u32[]{:S(2)}) collective-permute-start(bf16[8,64,128]{2,1,0:T(8,128)(2,1)S(1)} %get-tuple-element.47), channel_id=1, source_target_pairs={{0,6},{1,7},{2,4},{3,5},{4,2},{5,3},{6,0},{7,1},{8,14},{9,15},{10,... | collective-permute-start | bytes 393224 | tf_op jit(solution)/shard_map/ppermute | solution.py:37
  69.5 2.6 %collective-permute-done.30.refs_4_ = bf16[8,64,128]{2,1,0:T(8,128)(2,1)S(1)} collective-permute-done((bf16[8,64,128]{2,1,0:T(8,128)(2,1)S(1)}, bf16[8,64,128]{2,1,0:T(8,128)(2,1)S(1)}, u32[]{:S(2)}, u32[]{:S(2)}) %collective-permute-start.30) | collective-permute-done | bytes 131104 | tf_op jit(solution)/shard_map/ppermute | solution.py:37
  72.1 0.9 collective-permute-done.28.refs_2_
  73.0 0.8 shard_map.65
  73.8 2.3 %collective-permute-start.32 = (bf16[1,8,64,128]{3,2,1,0:T(8,128)(2,1)S(1)}, bf16[1,8,64,128]{3,2,1,0:T(8,128)(2,1)S(1)}, u32[]{:S(2)}, u32[]{:S(2)}) collective-permute-start(bf16[1,8,64,128]{3,2,1,0:T(8,128)(2,1)S(1)} %bitcast.38), channel_id=1, source_target_pairs={{0,16},{8,24},{16,0},{24,8},{1,17},{9,25},{17,1},{25,9},{2,18},{10... | collective-permute-start | bytes 393224 | tf_op jit(solution)/shard_map/ppermute | solution.py:37
  76.1 2.4 %collective-permute-start.36 = (bf16[8,64,128]{2,1,0:T(8,128)(2,1)S(1)}, bf16[8,64,128]{2,1,0:T(8,128)(2,1)S(1)}, u32[]{:S(2)}, u32[]{:S(2)}) collective-permute-start(bf16[8,64,128]{2,1,0:T(8,128)(2,1)S(1)} %get-tuple-element.53), channel_id=1, source_target_pairs={{0,6},{1,7},{2,4},{3,5},{4,2},{5,3},{6,0},{7,1},{8,14},{9,15},{10,... | collective-permute-start | bytes 393224 | tf_op jit(solution)/shard_map/ppermute | solution.py:37
  79.6 3.0 %collective-permute-done.32 = bf16[1,8,64,128]{3,2,1,0:T(8,128)(2,1)S(1)} collective-permute-done((bf16[1,8,64,128]{3,2,1,0:T(8,128)(2,1)S(1)}, bf16[1,8,64,128]{3,2,1,0:T(8,128)(2,1)S(1)}, u32[]{:S(2)}, u32[]{:S(2)}) %collective-permute-start.32) | collective-permute-done | bytes 131104 | tf_op jit(solution)/shard_map/ppermute | solution.py:37
  83.3 1.2 %collective-permute-done.35 = bf16[8,64,128]{2,1,0:T(8,128)(2,1)S(1)} collective-permute-done((bf16[8,64,128]{2,1,0:T(8,128)(2,1)S(1)}, bf16[8,64,128]{2,1,0:T(8,128)(2,1)S(1)}, u32[]{:S(2)}, u32[]{:S(2)}) %collective-permute-start.35) | collective-permute-done | bytes 131104 | tf_op jit(solution)/shard_map/ppermute | solution.py:37
  85.0 0.8 collective-permute-done.39
  86.0 3.0 %collective-permute-done.33.refs_1_ = bf16[2,8,64,128]{3,2,1,0:T(8,128)(2,1)S(1)} collective-permute-done((bf16[2,8,64,128]{3,2,1,0:T(8,128)(2,1)S(1)}, bf16[2,8,64,128]{3,2,1,0:T(8,128)(2,1)S(1)}, u32[]{:S(2)}, u32[]{:S(2)}) %collective-permute-start.33) | collective-permute-done | bytes 262176 | tf_op jit(solution)/shard_map/ppermute | solution.py:37
  89.1 2.3 %shard_map.66 = f32[40,128]{1,0:T(8,128)S(1)} custom-call(s32[2]{0:T(128)S(1)} %pad_add_fusion.meta, s32[32]{0:T(128)S(1)} %bitcast.64, s32[32]{0:T(128)S(1)} %bitcast.67, bf16[32,128,128]{2,1,0:T(8,128)(2,1)S(1)} %bitcast.31, f32[64,128]{1,0:T(8,128)S(1)} %get-tuple-element.52.gram_ref, bf16[2,8,64,128]{3,2,1,0:T(8,128)(2,1)S(1)} %pad_maximum_fusion.2.refs_0_, ...), custom_call_target="tpu_custom_call" | custom-call | flops 134217728 | bytes 2654472 | tf_op jit(solution)/shard_map/pallas_call | solution.py:24
  91.3 1.2 %collective-permute-done.41 = f32[40,128]{1,0:T(8,128)S(1)} collective-permute-done((f32[40,128]{1,0:T(8,128)S(1)}, f32[40,128]{1,0:T(8,128)S(1)}, u32[]{:S(2)}, u32[]{:S(2)}) %collective-permute-start.41) | collective-permute-done | bytes 20512 | tf_op jit(solution)/shard_map/ppermute | solution.py:37
  92.5 2.5 %collective-permute-start.44 = (f32[40,128]{1,0:T(8,128)S(1)}, f32[40,128]{1,0:T(8,128)S(1)}, u32[]{:S(2)}, u32[]{:S(2)}) collective-permute-start(f32[40,128]{1,0:T(8,128)S(1)} %add.12), channel_id=1, source_target_pairs={{0,6},{1,7},{2,4},{3,5},{4,2},{5,3},{6,0},{7,1},{8,14},{9,15},{10,... | collective-permute-start | bytes 61448 | tf_op jit(solution)/shard_map/ppermute | solution.py:37
  96.0 1.2 %collective-permute-done.44 = f32[40,128]{1,0:T(8,128)S(1)} collective-permute-done((f32[40,128]{1,0:T(8,128)S(1)}, f32[40,128]{1,0:T(8,128)S(1)}, u32[]{:S(2)}, u32[]{:S(2)}) %collective-permute-start.44) | collective-permute-done | bytes 20512 | tf_op jit(solution)/shard_map/ppermute | solution.py:37
  97.2 1.6 %collective-permute-done.43 = f32[40,128]{1,0:T(8,128)S(1)} collective-permute-done((f32[40,128]{1,0:T(8,128)S(1)}, f32[40,128]{1,0:T(8,128)S(1)}, u32[]{:S(2)}, u32[]{:S(2)}) %collective-permute-start.43) | collective-permute-done | bytes 20512 | tf_op jit(solution)/shard_map/ppermute | solution.py:37
  99.3 1.9 %collective-permute-start.47 = (f32[40,128]{1,0:T(8,128)S(1)}, f32[40,128]{1,0:T(8,128)S(1)}, u32[]{:S(2)}, u32[]{:S(2)}) collective-permute-start(f32[40,128]{1,0:T(8,128)S(1)} %add_add_fusion.refs_0_), channel_id=1, source_target_pairs={{0,24},{8,16},{16,8},{24,0},{1,25},{9,17},{17,9},{25,1},{2,26},{10... | collective-permute-start | bytes 61448 | tf_op jit(solution)/shard_map/ppermute | solution.py:37
  101.1 2.6 %collective-permute-start.45 = (f32[40,128]{1,0:T(8,128)S(1)}, f32[40,128]{1,0:T(8,128)S(1)}, u32[]{:S(2)}, u32[]{:S(2)}) collective-permute-start(f32[40,128]{1,0:T(8,128)S(1)} %add_add_fusion.refs_0_), channel_id=1, source_target_pairs={{0,8},{8,0},{16,24},{24,16},{1,9},{9,1},{17,25},{25,17},{2,10},{10... | collective-permute-start | bytes 61448 | tf_op jit(solution)/shard_map/ppermute | solution.py:37
  103.7 1.2 %collective-permute-done.47.refs_3_ = f32[40,128]{1,0:T(8,128)S(1)} collective-permute-done((f32[40,128]{1,0:T(8,128)S(1)}, f32[40,128]{1,0:T(8,128)S(1)}, u32[]{:S(2)}, u32[]{:S(2)}) %collective-permute-start.47) | collective-permute-done | bytes 20512 | tf_op jit(solution)/shard_map/ppermute | solution.py:37
  104.9 0.9 collective-permute-done.46.refs_2_
  105.8 7.2 %shard_map.67 = (f32[64,1024]{1,0:T(8,128)}, f32[64,64]{1,0:T(8,128)}) custom-call(f32[64,1024]{1,0:T(8,128)S(1)} %get-tuple-element.51.filtered_ref, f32[40,128]{1,0:T(8,128)S(1)} %add_add_fusion.refs_0_, f32[40,128]{1,0:T(8,128)S(1)} %collective-permute-done.45.refs_1_, f32[40,128]{1,0:T(8,128)S(1)} %collective-permute-done.46.refs_2_, ...), custom_call_target="tpu_custom_call" | custom-call | bytes 344064 | tf_op jit(solution)/shard_map/pallas_call | solution.py:24
  (79 shorter events, 11.2 us)
Async XLA Ops:
  1.6 10.4 %collective-permute-start = (bf16[1,8,64,128]{3,2,1,0:T(8,128)(2,1)S(1)}, bf16[1,8,64,128]{3,2,1,0:T(8,128)(2,1)S(1)}, u32[]{:S(2)}, u32[]{:S(2)}) collective-permute-start(bf16[1,8,64,128]{3,2,1,0:T(8,128)(2,1)S(1)} %bitcast.32), channel_id=1, source_target_pairs={{0,16},{8,24},{16,0},{24,8},{1,17},{9,25},{17,1},{25,9},{2,18},{10... | collective-permute-start | bytes 393224 | tf_op jit(solution)/shard_map/ppermute | solution.py:37
  5.7 7.1 %collective-permute-start.4 = (bf16[8,64,128]{2,1,0:T(8,128)(2,1)S(1)}, bf16[8,64,128]{2,1,0:T(8,128)(2,1)S(1)}, u32[]{:S(2)}, u32[]{:S(2)}) collective-permute-start(bf16[8,64,128]{2,1,0:T(8,128)(2,1)S(1)} %shard_map.59), channel_id=1, source_target_pairs={{0,6},{1,7},{2,4},{3,5},{4,2},{5,3},{6,0},{7,1},{8,14},{9,15},{10,... | collective-permute-start | bytes 393224 | tf_op jit(solution)/shard_map/ppermute | solution.py:37
  8.2 6.2 %collective-permute-start.3 = (bf16[8,64,128]{2,1,0:T(8,128)(2,1)S(1)}, bf16[8,64,128]{2,1,0:T(8,128)(2,1)S(1)}, u32[]{:S(2)}, u32[]{:S(2)}) collective-permute-start(bf16[8,64,128]{2,1,0:T(8,128)(2,1)S(1)} %shard_map.59), channel_id=1, source_target_pairs={{0,4},{1,5},{2,6},{3,7},{4,0},{5,1},{6,2},{7,3},{8,12},{9,13},{10,... | collective-permute-start | bytes 393224 | tf_op jit(solution)/shard_map/ppermute | solution.py:37
  8.7 5.8 %collective-permute-start.2 = (bf16[8,64,128]{2,1,0:T(8,128)(2,1)S(1)}, bf16[8,64,128]{2,1,0:T(8,128)(2,1)S(1)}, u32[]{:S(2)}, u32[]{:S(2)}) collective-permute-start(bf16[8,64,128]{2,1,0:T(8,128)(2,1)S(1)} %shard_map.59), channel_id=1, source_target_pairs={{0,2},{1,3},{2,0},{3,1},{4,6},{5,7},{6,4},{7,5},{8,10},{9,11},{10,... | collective-permute-start | bytes 393224 | tf_op jit(solution)/shard_map/ppermute | solution.py:37
  12.0 7.6 %collective-permute-start.1 = (bf16[2,8,64,128]{3,2,1,0:T(8,128)(2,1)S(1)}, bf16[2,8,64,128]{3,2,1,0:T(8,128)(2,1)S(1)}, u32[]{:S(2)}, u32[]{:S(2)}) collective-permute-start(bf16[2,8,64,128]{3,2,1,0:T(8,128)(2,1)S(1)} %pad_maximum_fusion.refs_0_), channel_id=1, source_target_pairs={{0,8},{8,0},{16,24},{24,16},{1,9},{9,1},{17,25},{25,17},{2,10},{10... | collective-permute-start | bytes 786440 | tf_op jit(solution)/shard_map/ppermute | solution.py:37
  12.8 2.1 %collective-permute-start.5 = (bf16[8,64,128]{2,1,0:T(8,128)(2,1)S(1)}, bf16[8,64,128]{2,1,0:T(8,128)(2,1)S(1)}, u32[]{:S(2)}, u32[]{:S(2)}) collective-permute-start(bf16[8,64,128]{2,1,0:T(8,128)(2,1)S(1)} %shard_map.59), channel_id=1, source_target_pairs={{0,1},{1,0},{2,3},{3,2},{4,5},{5,4},{6,7},{7,6},{8,9},{9,8},{10,11... | collective-permute-start | bytes 393224 | tf_op jit(solution)/shard_map/ppermute | solution.py:37
  12.8 2.1 %collective-permute-start.8 = (bf16[8,64,128]{2,1,0:T(8,128)(2,1)S(1)}, bf16[8,64,128]{2,1,0:T(8,128)(2,1)S(1)}, u32[]{:S(2)}, u32[]{:S(2)}) collective-permute-start(bf16[8,64,128]{2,1,0:T(8,128)(2,1)S(1)} %collective-permute-done.4), channel_id=1, source_target_pairs={{0,1},{1,0},{2,3},{3,2},{4,5},{5,4},{6,7},{7,6},{8,9},{9,8},{10,11... | collective-permute-start | bytes 393224 | tf_op jit(solution)/shard_map/ppermute | solution.py:37
  14.4 1.3 %collective-permute-start.7 = (bf16[8,64,128]{2,1,0:T(8,128)(2,1)S(1)}, bf16[8,64,128]{2,1,0:T(8,128)(2,1)S(1)}, u32[]{:S(2)}, u32[]{:S(2)}) collective-permute-start(bf16[8,64,128]{2,1,0:T(8,128)(2,1)S(1)} %collective-permute-done.3), channel_id=1, source_target_pairs={{0,1},{1,0},{2,3},{3,2},{4,5},{5,4},{6,7},{7,6},{8,9},{9,8},{10,11... | collective-permute-start | bytes 393224 | tf_op jit(solution)/shard_map/ppermute | solution.py:37
  14.4 1.5 %collective-permute-start.6 = (bf16[8,64,128]{2,1,0:T(8,128)(2,1)S(1)}, bf16[8,64,128]{2,1,0:T(8,128)(2,1)S(1)}, u32[]{:S(2)}, u32[]{:S(2)}) collective-permute-start(bf16[8,64,128]{2,1,0:T(8,128)(2,1)S(1)} %collective-permute-done.2), channel_id=1, source_target_pairs={{0,1},{1,0},{2,3},{3,2},{4,5},{5,4},{6,7},{7,6},{8,9},{9,8},{10,11... | collective-permute-start | bytes 393224 | tf_op jit(solution)/shard_map/ppermute | solution.py:37
  24.3 5.0 %collective-permute-start.9 = (bf16[4,9,64,128]{3,2,1,0:T(8,128)(2,1)S(1)}, bf16[4,9,64,128]{3,2,1,0:T(8,128)(2,1)S(1)}, u32[]{:S(2)}, u32[]{:S(2)}) collective-permute-start(bf16[4,9,64,128]{3,2,1,0:T(8,128)(2,1)S(1)} %get-tuple-element.29), channel_id=1, source_target_pairs={{0,1},{1,0},{2,3},{3,2},{4,5},{5,4},{6,7},{7,6},{8,9},{9,8},{10,11... | collective-permute-start | bytes 1769480 | tf_op jit(solution)/shard_map/ppermute | solution.py:37
  24.4 8.9 %collective-permute-start.13 = (bf16[9,64,128]{2,1,0:T(8,128)(2,1)S(1)}, bf16[9,64,128]{2,1,0:T(8,128)(2,1)S(1)}, u32[]{:S(2)}, u32[]{:S(2)}) collective-permute-start(bf16[9,64,128]{2,1,0:T(8,128)(2,1)S(1)} %get-tuple-element.35), channel_id=1, source_target_pairs={{0,8},{8,0},{16,24},{24,16},{1,9},{9,1},{17,25},{25,17},{2,10},{10... | collective-permute-start | bytes 442376 | tf_op jit(solution)/shard_map/ppermute | solution.py:37
  25.9 14.4 %collective-permute-start.14 = (bf16[9,64,128]{2,1,0:T(8,128)(2,1)S(1)}, bf16[9,64,128]{2,1,0:T(8,128)(2,1)S(1)}, u32[]{:S(2)}, u32[]{:S(2)}) collective-permute-start(bf16[9,64,128]{2,1,0:T(8,128)(2,1)S(1)} %get-tuple-element.36), channel_id=1, source_target_pairs={{0,16},{8,24},{16,0},{24,8},{1,17},{9,25},{17,1},{25,9},{2,18},{10... | collective-permute-start | bytes 442376 | tf_op jit(solution)/shard_map/ppermute | solution.py:37
  29.3 11.0 %collective-permute-start.15 = (bf16[9,64,128]{2,1,0:T(8,128)(2,1)S(1)}, bf16[9,64,128]{2,1,0:T(8,128)(2,1)S(1)}, u32[]{:S(2)}, u32[]{:S(2)}) collective-permute-start(bf16[9,64,128]{2,1,0:T(8,128)(2,1)S(1)} %get-tuple-element.37), channel_id=1, source_target_pairs={{0,24},{8,16},{16,8},{24,0},{1,25},{9,17},{17,9},{25,1},{2,26},{10... | collective-permute-start | bytes 442376 | tf_op jit(solution)/shard_map/ppermute | solution.py:37
  29.5 10.8 %collective-permute-start.10 = (bf16[9,64,128]{2,1,0:T(8,128)(2,1)S(1)}, bf16[9,64,128]{2,1,0:T(8,128)(2,1)S(1)}, u32[]{:S(2)}, u32[]{:S(2)}) collective-permute-start(bf16[9,64,128]{2,1,0:T(8,128)(2,1)S(1)} %get-tuple-element.32), channel_id=1, source_target_pairs={{0,2},{1,3},{2,0},{3,1},{4,6},{5,7},{6,4},{7,5},{8,10},{9,11},{10,... | collective-permute-start | bytes 442376 | tf_op jit(solution)/shard_map/ppermute | solution.py:37
  31.0 9.3 %collective-permute-start.11 = (bf16[9,64,128]{2,1,0:T(8,128)(2,1)S(1)}, bf16[9,64,128]{2,1,0:T(8,128)(2,1)S(1)}, u32[]{:S(2)}, u32[]{:S(2)}) collective-permute-start(bf16[9,64,128]{2,1,0:T(8,128)(2,1)S(1)} %get-tuple-element.33), channel_id=1, source_target_pairs={{0,4},{1,5},{2,6},{3,7},{4,0},{5,1},{6,2},{7,3},{8,12},{9,13},{10,... | collective-permute-start | bytes 442376 | tf_op jit(solution)/shard_map/ppermute | solution.py:37
  33.3 7.0 %collective-permute-start.12 = (bf16[9,64,128]{2,1,0:T(8,128)(2,1)S(1)}, bf16[9,64,128]{2,1,0:T(8,128)(2,1)S(1)}, u32[]{:S(2)}, u32[]{:S(2)}) collective-permute-start(bf16[9,64,128]{2,1,0:T(8,128)(2,1)S(1)} %get-tuple-element.34), channel_id=1, source_target_pairs={{0,6},{1,7},{2,4},{3,5},{4,2},{5,3},{6,0},{7,1},{8,14},{9,15},{10,... | collective-permute-start | bytes 442376 | tf_op jit(solution)/shard_map/ppermute | solution.py:37
  40.5 10.1 %collective-permute-start.16 = (bf16[1,8,64,128]{3,2,1,0:T(8,128)(2,1)S(1)}, bf16[1,8,64,128]{3,2,1,0:T(8,128)(2,1)S(1)}, u32[]{:S(2)}, u32[]{:S(2)}) collective-permute-start(bf16[1,8,64,128]{3,2,1,0:T(8,128)(2,1)S(1)} %bitcast.35), channel_id=1, source_target_pairs={{0,16},{8,24},{16,0},{24,8},{1,17},{9,25},{17,1},{25,9},{2,18},{10... | collective-permute-start | bytes 393224 | tf_op jit(solution)/shard_map/ppermute | solution.py:37
  44.8 6.8 %collective-permute-start.20 = (bf16[8,64,128]{2,1,0:T(8,128)(2,1)S(1)}, bf16[8,64,128]{2,1,0:T(8,128)(2,1)S(1)}, u32[]{:S(2)}, u32[]{:S(2)}) collective-permute-start(bf16[8,64,128]{2,1,0:T(8,128)(2,1)S(1)} %get-tuple-element.40), channel_id=1, source_target_pairs={{0,6},{1,7},{2,4},{3,5},{4,2},{5,3},{6,0},{7,1},{8,14},{9,15},{10,... | collective-permute-start | bytes 393224 | tf_op jit(solution)/shard_map/ppermute | solution.py:37
  47.2 5.7 %collective-permute-start.19 = (bf16[8,64,128]{2,1,0:T(8,128)(2,1)S(1)}, bf16[8,64,128]{2,1,0:T(8,128)(2,1)S(1)}, u32[]{:S(2)}, u32[]{:S(2)}) collective-permute-start(bf16[8,64,128]{2,1,0:T(8,128)(2,1)S(1)} %get-tuple-element.40), channel_id=1, source_target_pairs={{0,4},{1,5},{2,6},{3,7},{4,0},{5,1},{6,2},{7,3},{8,12},{9,13},{10,... | collective-permute-start | bytes 393224 | tf_op jit(solution)/shard_map/ppermute | solution.py:37
  47.7 5.3 %collective-permute-start.18 = (bf16[8,64,128]{2,1,0:T(8,128)(2,1)S(1)}, bf16[8,64,128]{2,1,0:T(8,128)(2,1)S(1)}, u32[]{:S(2)}, u32[]{:S(2)}) collective-permute-start(bf16[8,64,128]{2,1,0:T(8,128)(2,1)S(1)} %get-tuple-element.40), channel_id=1, source_target_pairs={{0,2},{1,3},{2,0},{3,1},{4,6},{5,7},{6,4},{7,5},{8,10},{9,11},{10,... | collective-permute-start | bytes 393224 | tf_op jit(solution)/shard_map/ppermute | solution.py:37
  50.7 6.4 %collective-permute-start.17 = (bf16[2,8,64,128]{3,2,1,0:T(8,128)(2,1)S(1)}, bf16[2,8,64,128]{3,2,1,0:T(8,128)(2,1)S(1)}, u32[]{:S(2)}, u32[]{:S(2)}) collective-permute-start(bf16[2,8,64,128]{3,2,1,0:T(8,128)(2,1)S(1)} %pad_maximum_fusion.1.refs_0_), channel_id=1, source_target_pairs={{0,8},{8,0},{16,24},{24,16},{1,9},{9,1},{17,25},{25,17},{2,10},{10... | collective-permute-start | bytes 786440 | tf_op jit(solution)/shard_map/ppermute | solution.py:37
  50.8 2.7 %collective-permute-start.21 = (bf16[8,64,128]{2,1,0:T(8,128)(2,1)S(1)}, bf16[8,64,128]{2,1,0:T(8,128)(2,1)S(1)}, u32[]{:S(2)}, u32[]{:S(2)}) collective-permute-start(bf16[8,64,128]{2,1,0:T(8,128)(2,1)S(1)} %get-tuple-element.40), channel_id=1, source_target_pairs={{0,1},{1,0},{2,3},{3,2},{4,5},{5,4},{6,7},{7,6},{8,9},{9,8},{10,11... | collective-permute-start | bytes 393224 | tf_op jit(solution)/shard_map/ppermute | solution.py:37
  51.5 1.9 %collective-permute-start.24 = (bf16[8,64,128]{2,1,0:T(8,128)(2,1)S(1)}, bf16[8,64,128]{2,1,0:T(8,128)(2,1)S(1)}, u32[]{:S(2)}, u32[]{:S(2)}) collective-permute-start(bf16[8,64,128]{2,1,0:T(8,128)(2,1)S(1)} %collective-permute-done.20), channel_id=1, source_target_pairs={{0,1},{1,0},{2,3},{3,2},{4,5},{5,4},{6,7},{7,6},{8,9},{9,8},{10,11... | collective-permute-start | bytes 393224 | tf_op jit(solution)/shard_map/ppermute | solution.py:37
  52.9 1.3 %collective-permute-start.23 = (bf16[8,64,128]{2,1,0:T(8,128)(2,1)S(1)}, bf16[8,64,128]{2,1,0:T(8,128)(2,1)S(1)}, u32[]{:S(2)}, u32[]{:S(2)}) collective-permute-start(bf16[8,64,128]{2,1,0:T(8,128)(2,1)S(1)} %collective-permute-done.19), channel_id=1, source_target_pairs={{0,1},{1,0},{2,3},{3,2},{4,5},{5,4},{6,7},{7,6},{8,9},{9,8},{10,11... | collective-permute-start | bytes 393224 | tf_op jit(solution)/shard_map/ppermute | solution.py:37
  53.0 1.4 %collective-permute-start.22 = (bf16[8,64,128]{2,1,0:T(8,128)(2,1)S(1)}, bf16[8,64,128]{2,1,0:T(8,128)(2,1)S(1)}, u32[]{:S(2)}, u32[]{:S(2)}) collective-permute-start(bf16[8,64,128]{2,1,0:T(8,128)(2,1)S(1)} %collective-permute-done.18), channel_id=1, source_target_pairs={{0,1},{1,0},{2,3},{3,2},{4,5},{5,4},{6,7},{7,6},{8,9},{9,8},{10,11... | collective-permute-start | bytes 393224 | tf_op jit(solution)/shard_map/ppermute | solution.py:37
  59.0 4.5 %collective-permute-start.25 = (bf16[4,8,64,128]{3,2,1,0:T(8,128)(2,1)S(1)}, bf16[4,8,64,128]{3,2,1,0:T(8,128)(2,1)S(1)}, u32[]{:S(2)}, u32[]{:S(2)}) collective-permute-start(bf16[4,8,64,128]{3,2,1,0:T(8,128)(2,1)S(1)} %get-tuple-element.42), channel_id=1, source_target_pairs={{0,1},{1,0},{2,3},{3,2},{4,5},{5,4},{6,7},{7,6},{8,9},{9,8},{10,11... | collective-permute-start | bytes 1572872 | tf_op jit(solution)/shard_map/ppermute | solution.py:37
  59.1 7.9 %collective-permute-start.29 = (bf16[8,64,128]{2,1,0:T(8,128)(2,1)S(1)}, bf16[8,64,128]{2,1,0:T(8,128)(2,1)S(1)}, u32[]{:S(2)}, u32[]{:S(2)}) collective-permute-start(bf16[8,64,128]{2,1,0:T(8,128)(2,1)S(1)} %get-tuple-element.48), channel_id=1, source_target_pairs={{0,8},{8,0},{16,24},{24,16},{1,9},{9,1},{17,25},{25,17},{2,10},{10... | collective-permute-start | bytes 393224 | tf_op jit(solution)/shard_map/ppermute | solution.py:37
  59.2 12.9 %collective-permute-start.30 = (bf16[8,64,128]{2,1,0:T(8,128)(2,1)S(1)}, bf16[8,64,128]{2,1,0:T(8,128)(2,1)S(1)}, u32[]{:S(2)}, u32[]{:S(2)}) collective-permute-start(bf16[8,64,128]{2,1,0:T(8,128)(2,1)S(1)} %get-tuple-element.49), channel_id=1, source_target_pairs={{0,16},{8,24},{16,0},{24,8},{1,17},{9,25},{17,1},{25,9},{2,18},{10... | collective-permute-start | bytes 393224 | tf_op jit(solution)/shard_map/ppermute | solution.py:37
  61.5 10.6 %collective-permute-start.31 = (bf16[8,64,128]{2,1,0:T(8,128)(2,1)S(1)}, bf16[8,64,128]{2,1,0:T(8,128)(2,1)S(1)}, u32[]{:S(2)}, u32[]{:S(2)}) collective-permute-start(bf16[8,64,128]{2,1,0:T(8,128)(2,1)S(1)} %get-tuple-element.50), channel_id=1, source_target_pairs={{0,24},{8,16},{16,8},{24,0},{1,25},{9,17},{17,9},{25,1},{2,26},{10... | collective-permute-start | bytes 393224 | tf_op jit(solution)/shard_map/ppermute | solution.py:37
  63.7 8.5 %collective-permute-start.26 = (bf16[8,64,128]{2,1,0:T(8,128)(2,1)S(1)}, bf16[8,64,128]{2,1,0:T(8,128)(2,1)S(1)}, u32[]{:S(2)}, u32[]{:S(2)}) collective-permute-start(bf16[8,64,128]{2,1,0:T(8,128)(2,1)S(1)} %get-tuple-element.45), channel_id=1, source_target_pairs={{0,2},{1,3},{2,0},{3,1},{4,6},{5,7},{6,4},{7,5},{8,10},{9,11},{10,... | collective-permute-start | bytes 393224 | tf_op jit(solution)/shard_map/ppermute | solution.py:37
  65.2 6.9 %collective-permute-start.27 = (bf16[8,64,128]{2,1,0:T(8,128)(2,1)S(1)}, bf16[8,64,128]{2,1,0:T(8,128)(2,1)S(1)}, u32[]{:S(2)}, u32[]{:S(2)}) collective-permute-start(bf16[8,64,128]{2,1,0:T(8,128)(2,1)S(1)} %get-tuple-element.46), channel_id=1, source_target_pairs={{0,4},{1,5},{2,6},{3,7},{4,0},{5,1},{6,2},{7,3},{8,12},{9,13},{10,... | collective-permute-start | bytes 393224 | tf_op jit(solution)/shard_map/ppermute | solution.py:37
  67.0 6.0 %collective-permute-start.28 = (bf16[8,64,128]{2,1,0:T(8,128)(2,1)S(1)}, bf16[8,64,128]{2,1,0:T(8,128)(2,1)S(1)}, u32[]{:S(2)}, u32[]{:S(2)}) collective-permute-start(bf16[8,64,128]{2,1,0:T(8,128)(2,1)S(1)} %get-tuple-element.47), channel_id=1, source_target_pairs={{0,6},{1,7},{2,4},{3,5},{4,2},{5,3},{6,0},{7,1},{8,14},{9,15},{10,... | collective-permute-start | bytes 393224 | tf_op jit(solution)/shard_map/ppermute | solution.py:37
  73.8 8.8 %collective-permute-start.32 = (bf16[1,8,64,128]{3,2,1,0:T(8,128)(2,1)S(1)}, bf16[1,8,64,128]{3,2,1,0:T(8,128)(2,1)S(1)}, u32[]{:S(2)}, u32[]{:S(2)}) collective-permute-start(bf16[1,8,64,128]{3,2,1,0:T(8,128)(2,1)S(1)} %bitcast.38), channel_id=1, source_target_pairs={{0,16},{8,24},{16,0},{24,8},{1,17},{9,25},{17,1},{25,9},{2,18},{10... | collective-permute-start | bytes 393224 | tf_op jit(solution)/shard_map/ppermute | solution.py:37
  76.1 6.7 %collective-permute-start.36 = (bf16[8,64,128]{2,1,0:T(8,128)(2,1)S(1)}, bf16[8,64,128]{2,1,0:T(8,128)(2,1)S(1)}, u32[]{:S(2)}, u32[]{:S(2)}) collective-permute-start(bf16[8,64,128]{2,1,0:T(8,128)(2,1)S(1)} %get-tuple-element.53), channel_id=1, source_target_pairs={{0,6},{1,7},{2,4},{3,5},{4,2},{5,3},{6,0},{7,1},{8,14},{9,15},{10,... | collective-permute-start | bytes 393224 | tf_op jit(solution)/shard_map/ppermute | solution.py:37
  78.6 5.9 %collective-permute-start.35 = (bf16[8,64,128]{2,1,0:T(8,128)(2,1)S(1)}, bf16[8,64,128]{2,1,0:T(8,128)(2,1)S(1)}, u32[]{:S(2)}, u32[]{:S(2)}) collective-permute-start(bf16[8,64,128]{2,1,0:T(8,128)(2,1)S(1)} %get-tuple-element.53), channel_id=1, source_target_pairs={{0,4},{1,5},{2,6},{3,7},{4,0},{5,1},{6,2},{7,3},{8,12},{9,13},{10,... | collective-permute-start | bytes 393224 | tf_op jit(solution)/shard_map/ppermute | solution.py:37
  79.1 5.5 %collective-permute-start.34 = (bf16[8,64,128]{2,1,0:T(8,128)(2,1)S(1)}, bf16[8,64,128]{2,1,0:T(8,128)(2,1)S(1)}, u32[]{:S(2)}, u32[]{:S(2)}) collective-permute-start(bf16[8,64,128]{2,1,0:T(8,128)(2,1)S(1)} %get-tuple-element.53), channel_id=1, source_target_pairs={{0,2},{1,3},{2,0},{3,1},{4,6},{5,7},{6,4},{7,5},{8,10},{9,11},{10,... | collective-permute-start | bytes 393224 | tf_op jit(solution)/shard_map/ppermute | solution.py:37
  82.6 6.4 %collective-permute-start.33 = (bf16[2,8,64,128]{3,2,1,0:T(8,128)(2,1)S(1)}, bf16[2,8,64,128]{3,2,1,0:T(8,128)(2,1)S(1)}, u32[]{:S(2)}, u32[]{:S(2)}) collective-permute-start(bf16[2,8,64,128]{3,2,1,0:T(8,128)(2,1)S(1)} %pad_maximum_fusion.2.refs_0_), channel_id=1, source_target_pairs={{0,8},{8,0},{16,24},{24,16},{1,9},{9,1},{17,25},{25,17},{2,10},{10... | collective-permute-start | bytes 786440 | tf_op jit(solution)/shard_map/ppermute | solution.py:37
  82.7 2.3 %collective-permute-start.37 = (bf16[8,64,128]{2,1,0:T(8,128)(2,1)S(1)}, bf16[8,64,128]{2,1,0:T(8,128)(2,1)S(1)}, u32[]{:S(2)}, u32[]{:S(2)}) collective-permute-start(bf16[8,64,128]{2,1,0:T(8,128)(2,1)S(1)} %get-tuple-element.53), channel_id=1, source_target_pairs={{0,1},{1,0},{2,3},{3,2},{4,5},{5,4},{6,7},{7,6},{8,9},{9,8},{10,11... | collective-permute-start | bytes 393224 | tf_op jit(solution)/shard_map/ppermute | solution.py:37
  82.8 2.2 %collective-permute-start.40 = (bf16[8,64,128]{2,1,0:T(8,128)(2,1)S(1)}, bf16[8,64,128]{2,1,0:T(8,128)(2,1)S(1)}, u32[]{:S(2)}, u32[]{:S(2)}) collective-permute-start(bf16[8,64,128]{2,1,0:T(8,128)(2,1)S(1)} %collective-permute-done.36), channel_id=1, source_target_pairs={{0,1},{1,0},{2,3},{3,2},{4,5},{5,4},{6,7},{7,6},{8,9},{9,8},{10,11... | collective-permute-start | bytes 393224 | tf_op jit(solution)/shard_map/ppermute | solution.py:37
  84.5 1.3 %collective-permute-start.39 = (bf16[8,64,128]{2,1,0:T(8,128)(2,1)S(1)}, bf16[8,64,128]{2,1,0:T(8,128)(2,1)S(1)}, u32[]{:S(2)}, u32[]{:S(2)}) collective-permute-start(bf16[8,64,128]{2,1,0:T(8,128)(2,1)S(1)} %collective-permute-done.35), channel_id=1, source_target_pairs={{0,1},{1,0},{2,3},{3,2},{4,5},{5,4},{6,7},{7,6},{8,9},{9,8},{10,11... | collective-permute-start | bytes 393224 | tf_op jit(solution)/shard_map/ppermute | solution.py:37
  84.6 1.4 %collective-permute-start.38 = (bf16[8,64,128]{2,1,0:T(8,128)(2,1)S(1)}, bf16[8,64,128]{2,1,0:T(8,128)(2,1)S(1)}, u32[]{:S(2)}, u32[]{:S(2)}) collective-permute-start(bf16[8,64,128]{2,1,0:T(8,128)(2,1)S(1)} %collective-permute-done.34), channel_id=1, source_target_pairs={{0,1},{1,0},{2,3},{3,2},{4,5},{5,4},{6,7},{7,6},{8,9},{9,8},{10,11... | collective-permute-start | bytes 393224 | tf_op jit(solution)/shard_map/ppermute | solution.py:37
  91.3 1.2 %collective-permute-start.41 = (f32[40,128]{1,0:T(8,128)S(1)}, f32[40,128]{1,0:T(8,128)S(1)}, u32[]{:S(2)}, u32[]{:S(2)}) collective-permute-start(f32[40,128]{1,0:T(8,128)S(1)} %shard_map.66), channel_id=1, source_target_pairs={{0,1},{1,0},{2,3},{3,2},{4,5},{5,4},{6,7},{7,6},{8,9},{9,8},{10,11... | collective-permute-start | bytes 61448 | tf_op jit(solution)/shard_map/ppermute | solution.py:37
  92.5 4.7 %collective-permute-start.44 = (f32[40,128]{1,0:T(8,128)S(1)}, f32[40,128]{1,0:T(8,128)S(1)}, u32[]{:S(2)}, u32[]{:S(2)}) collective-permute-start(f32[40,128]{1,0:T(8,128)S(1)} %add.12), channel_id=1, source_target_pairs={{0,6},{1,7},{2,4},{3,5},{4,2},{5,3},{6,0},{7,1},{8,14},{9,15},{10,... | collective-permute-start | bytes 61448 | tf_op jit(solution)/shard_map/ppermute | solution.py:37
  95.0 3.8 %collective-permute-start.43 = (f32[40,128]{1,0:T(8,128)S(1)}, f32[40,128]{1,0:T(8,128)S(1)}, u32[]{:S(2)}, u32[]{:S(2)}) collective-permute-start(f32[40,128]{1,0:T(8,128)S(1)} %add.12), channel_id=1, source_target_pairs={{0,4},{1,5},{2,6},{3,7},{4,0},{5,1},{6,2},{7,3},{8,12},{9,13},{10,... | collective-permute-start | bytes 61448 | tf_op jit(solution)/shard_map/ppermute | solution.py:37
  95.5 3.8 %collective-permute-start.42 = (f32[40,128]{1,0:T(8,128)S(1)}, f32[40,128]{1,0:T(8,128)S(1)}, u32[]{:S(2)}, u32[]{:S(2)}) collective-permute-start(f32[40,128]{1,0:T(8,128)S(1)} %add.12), channel_id=1, source_target_pairs={{0,2},{1,3},{2,0},{3,1},{4,6},{5,7},{6,4},{7,5},{8,10},{9,11},{10,... | collective-permute-start | bytes 61448 | tf_op jit(solution)/shard_map/ppermute | solution.py:37
  99.3 5.6 %collective-permute-start.47 = (f32[40,128]{1,0:T(8,128)S(1)}, f32[40,128]{1,0:T(8,128)S(1)}, u32[]{:S(2)}, u32[]{:S(2)}) collective-permute-start(f32[40,128]{1,0:T(8,128)S(1)} %add_add_fusion.refs_0_), channel_id=1, source_target_pairs={{0,24},{8,16},{16,8},{24,0},{1,25},{9,17},{17,9},{25,1},{2,26},{10... | collective-permute-start | bytes 61448 | tf_op jit(solution)/shard_map/ppermute | solution.py:37
  101.1 4.7 %collective-permute-start.46 = (f32[40,128]{1,0:T(8,128)S(1)}, f32[40,128]{1,0:T(8,128)S(1)}, u32[]{:S(2)}, u32[]{:S(2)}) collective-permute-start(f32[40,128]{1,0:T(8,128)S(1)} %add_add_fusion.refs_0_), channel_id=1, source_target_pairs={{0,16},{8,24},{16,0},{24,8},{1,17},{9,25},{17,1},{25,9},{2,18},{10... | collective-permute-start | bytes 61448 | tf_op jit(solution)/shard_map/ppermute | solution.py:37
  101.1 4.7 %collective-permute-start.45 = (f32[40,128]{1,0:T(8,128)S(1)}, f32[40,128]{1,0:T(8,128)S(1)}, u32[]{:S(2)}, u32[]{:S(2)}) collective-permute-start(f32[40,128]{1,0:T(8,128)S(1)} %add_add_fusion.refs_0_), channel_id=1, source_target_pairs={{0,8},{8,0},{16,24},{24,16},{1,9},{9,1},{17,25},{25,17},{2,10},{10... | collective-permute-start | bytes 61448 | tf_op jit(solution)/shard_map/ppermute | solution.py:37
  (8 other events, 102.6 us)

commit v7 on v6

v7 whole, which is shorter than its diff:
```python
import functools

import jax
import jax.numpy as jnp
from jax import lax
from jax.experimental import pallas as pl
from jax.experimental.pallas import tpu as pltpu
from jax.sharding import PartitionSpec as P

CENTER = 1.0
HALF_WIDTH = 0.5
HIGHEST = lax.Precision.HIGHEST
NT = (((1,), (1,)), ((), ()))
NN = (((1,), (0,)), ((), ()))
BF16 = jnp.bfloat16
F32 = jnp.float32
VMEM = pl.BlockSpec(memory_space=pltpu.VMEM)
SMEM = pl.BlockSpec(memory_space=pltpu.SMEM)
DEGREE_ROWS = 16


def call(kernel, out_shape, scratch, limit, args, flops=0, smem=0):
    moved = sum(x.size * x.dtype.itemsize for x in args)
    return pl.pallas_call(
        kernel,
        out_shape=out_shape,
        in_specs=[SMEM] * smem + [VMEM] * (len(args) - smem),
        out_specs=jax.tree.map(lambda _: VMEM, out_shape),
        scratch_shapes=scratch,
        compiler_params=pltpu.CompilerParams(vmem_limit_bytes=limit * 2**20),
        cost_estimate=pl.CostEstimate(flops=flops, bytes_accessed=moved, transcendentals=0),
    )(*args)


def trade(part, axis, d):
    n = lax.axis_size(axis)
    return lax.ppermute(part, axis, [(i, i ^ d) for i in range(n)])


def exchange(parts, axis, step=1):
    far_first = [trade(part, axis, step * d) for d, part in reversed(list(enumerate(parts, 1)))]
    return far_first[::-1]


def tiles_first(ref, width):
    return [ref[:, k * width : (k + 1) * width] for k in range(ref.shape[1] // width)]


def round_kernel(vec_ref, out_ref):
    for k, piece in enumerate(tiles_first(vec_ref, out_ref.shape[2])):
        out_ref[k] = piece.astype(BF16)


def split_degree(sums):
    high = sums.astype(BF16).astype(F32)
    return jnp.concatenate([high, sums - high], 0).astype(BF16)


def join_degree(payload, group):
    parts = payload[payload.shape[0] - 2 * group :, :].astype(F32)
    return parts[:group] + parts[group:]


def fill(panel, parts, offsets):
    for part, offset in zip(parts, offsets):
        group = part.shape[0]
        panel[offset * group : (offset + 1) * group] = part[...]


def degree_kernel(table, tiles_ref, row_ref, col_ref):
    row_ref[...] = jnp.zeros_like(row_ref)
    col_ref[...] = jnp.zeros_like(col_ref)
    ones = jnp.ones((DEGREE_ROWS, tiles_ref.shape[2]), BF16)
    for t in range(tiles_ref.shape[0]):
        for ref, place, dims in ((row_ref, table[2, t], NT), (col_ref, table[0, t], NN)):
            sums = lax.dot_general(ones, tiles_ref[t], dims, preferred_element_type=F32)
            ref[pl.ds(place, 1), :] += sums[:1]


def product_kernel(offsets, degree, table, tiles_ref, *refs):
    col_offsets, row_offsets = offsets
    cols_n, rows_n = len(col_offsets), len(row_offsets)
    half = rows_n // 2
    col_parts, refs = refs[:cols_n], refs[cols_n:]
    row_parts, refs = refs[:rows_n], refs[rows_n:]
    if degree:
        row_degree, col_degree, *refs = refs
    kept_ref, swap_ref, own_ref, *send_refs = refs[:-4]
    col_panel, row_panel, row_total, col_total = refs[-4:]
    group, vectors_n, width = col_parts[0].shape
    fill(col_panel, col_parts, col_offsets)
    fill(row_panel, row_parts, row_offsets)
    row_total[...] = jnp.zeros_like(row_total)
    col_total[...] = jnp.zeros_like(col_total)
    for t in range(tiles_ref.shape[0]):
        tile, here = tiles_ref[t], table[0, t]
        row_total[table[2, t]] += lax.dot_general(
            col_panel[here], tile, NT, preferred_element_type=F32
        )
        col_total[here] += lax.dot_general(
            row_panel[table[1, t]], tile, NN, preferred_element_type=F32
        )
    for d in range(half):
        kept_ref[d] = row_total[d * group : (d + 1) * group]
    own_ref[...] = col_total[:group]
    sends = [(row_total, half + d, swap_ref.at[d]) for d in range(half)]
    sends += [(col_total, d, send) for d, send in enumerate(send_refs, 1)]
    for total, d, send in sends:
        for k in range(group):
            send[k * vectors_n : (k + 1) * vectors_n, :] = total[d * group + k].astype(BF16)
        if degree:
            sums = row_degree if total is row_total else col_degree
            send[group * vectors_n :, :] = split_degree(sums[d * group : (d + 1) * group, :])


def products(tiles, table, col_parts, row_parts, offsets, degree):
    group, vectors_n, width = col_parts[0].shape
    rows_n, half = len(offsets[0]), len(offsets[1]) // 2
    rows = group * vectors_n + (2 * group if degree else 0)
    out_shape = [
        jax.ShapeDtypeStruct((half, group, vectors_n, width), F32),
        jax.ShapeDtypeStruct((half, rows, width), BF16),
        jax.ShapeDtypeStruct((group, vectors_n, width), F32),
    ]
    out_shape += [jax.ShapeDtypeStruct((rows, width), BF16)] * (rows_n - 1)
    scratch = [
        pltpu.VMEM((rows_n * group, vectors_n, width), BF16),
        pltpu.VMEM((2 * half * group, vectors_n, width), BF16),
        pltpu.VMEM((2 * half * group, vectors_n, width), F32),
        pltpu.VMEM((rows_n * group, vectors_n, width), F32),
    ]
    kernel = functools.partial(product_kernel, offsets, bool(degree))
    args = [table, tiles, *col_parts, *row_parts, *degree]
    kept, swap, own, *send = call(
        kernel, out_shape, scratch, 32, args, 4 * tiles.size * vectors_n, 1
    )
    return kept, swap, own, send


def merge_kernel(degree, kept, got, *refs):
    if degree:
        row_degree, own_ref, own_degree, *send_refs = refs
    else:
        own_ref, *send_refs = refs
    _, group, vectors_n, _ = kept.shape
    for k in range(group):
        rows = slice(k * vectors_n, (k + 1) * vectors_n)
        own_ref[k] = kept[0, k] + got[0, rows, :].astype(F32)
        for d, send in enumerate(send_refs, 1):
            send[rows, :] = (kept[d, k] + got[d, rows, :].astype(F32)).astype(BF16)
    if degree:
        for d in range(kept.shape[0]):
            sums = row_degree[d * group : (d + 1) * group, :] + join_degree(got.at[d], group)
            if d:
                send_refs[d - 1][group * vectors_n :, :] = split_degree(sums)
            else:
                own_degree[...] = sums


def merge(kept, got, degree):
    _, group, _, width = kept.shape
    out_shape = [jax.ShapeDtypeStruct(kept.shape[1:], F32)]
    if degree:
        out_shape += [jax.ShapeDtypeStruct((group, width), F32)]
    out_shape += [jax.ShapeDtypeStruct(got.shape[1:], BF16)] * (kept.shape[0] - 1)
    kernel = functools.partial(merge_kernel, bool(degree))
    return call(kernel, out_shape, [], 24, [kept, got, *degree[:1]])


def gathered_sum(own, received, k):
    total = own[k]
    rows = slice(k * total.shape[0], (k + 1) * total.shape[0])
    for part in received:
        total = total + part[rows, :].astype(F32)
    return total


def symmetric_part(row_own, row_refs, col_own, col_refs, k):
    return 0.5 * (gathered_sum(row_own, row_refs, k) + gathered_sum(col_own, col_refs, k))


def first_kernel(chips_n, vec_ref, row_degree, col_degree, row_own, col_own, *refs):
    row_refs, refs = refs[: chips_n - 1], refs[chips_n - 1 :]
    col_refs, (first_ref, rounded_ref, degree_ref) = refs[:-3], refs[-3:]
    group, _, width = rounded_ref.shape
    degree = row_degree[...] + col_degree[:group, :]
    for part in (*row_refs, *col_refs):
        degree += join_degree(part, group)
    degree = 0.5 * degree
    degree_ref[...] = degree
    for k, vec in enumerate(tiles_first(vec_ref, width)):
        symmetric = symmetric_part(row_own, row_refs, col_own, col_refs, k)
        image = degree[k : k + 1, :] * vec - symmetric
        first = (image - CENTER * vec) / HALF_WIDTH
        first_ref[:, k * width : (k + 1) * width] = first
        rounded_ref[k] = first.astype(BF16)


def filter_kernel(chips_n, start_ref, first_ref, degree_ref, row_own, col_own, *refs):
    row_refs, refs = refs[: chips_n - 1], refs[chips_n - 1 :]
    col_refs, (filtered_ref, rounded_ref, gram_ref, both) = refs[:-4], refs[-4:]
    group, vectors_n, width = rounded_ref.shape
    for k, vec in enumerate(tiles_first(first_ref, width)):
        symmetric = symmetric_part(row_own, row_refs, col_own, col_refs, k)
        columns = slice(k * width, (k + 1) * width)
        image = degree_ref[k : k + 1, :] * vec - symmetric
        filtered = 2.0 * (image - CENTER * vec) / HALF_WIDTH - start_ref[:, columns]
        filtered_ref[:, columns] = filtered
        rounded_ref[k] = filtered.astype(BF16)
        both[:vectors_n, columns] = filtered
        both[vectors_n:, columns] = degree_ref[k : k + 1, :] * filtered
    gram_ref[...] = lax.dot_general(
        filtered_ref[...], both[...], NT, precision=HIGHEST, preferred_element_type=F32
    )


def form_kernel(offsets, table, tiles_ref, gram_ref, *refs):
    col_end = len(offsets[0])
    col_parts, row_parts = refs[:col_end], refs[col_end:-5]
    out_ref, col_panel, row_panel, left, right = refs[-5:]
    _, vectors_n, width = col_panel.shape
    fill(col_panel, col_parts, offsets[0])
    fill(row_panel, row_parts, offsets[1])
    for t in range(tiles_ref.shape[0]):
        columns = slice(t * width, (t + 1) * width)
        left[:, columns] = row_panel[table[1, t]]
        right[:, columns] = lax.dot_general(
            col_panel[table[0, t]], tiles_ref[t], NT, preferred_element_type=F32
        ).astype(BF16)
    form = lax.dot_general(left[...], right[...], NT, preferred_element_type=F32)
    projected = gram_ref[:, vectors_n:] - 0.5 * (form + form.T)
    row, col = square_index(vectors_n)
    packed = jnp.where(col >= row, gram_ref[:, :vectors_n], projected)
    diagonal = jnp.sum(jnp.where(row == col, projected, 0.0), 0, keepdims=True)
    half = vectors_n // 2
    out_ref[:half] = jnp.concatenate([packed[:half], packed[half:]], 1)
    diagonal = jnp.broadcast_to(diagonal, (8, vectors_n))
    out_ref[half:] = jnp.concatenate([diagonal, jnp.zeros_like(diagonal)], 1)


def square_index(n):
    return tuple(lax.broadcasted_iota(jnp.int32, (n, n), axis) for axis in (0, 1))


def inverse_factor(gram):
    n = gram.shape[0]
    row, col = square_index(n)
    table = jnp.concatenate([gram, jnp.where(row == col, 1.0, 0.0)], 1)
    bands = [table[i : i + 8] for i in range(0, n, 8)]
    line = lax.broadcasted_iota(jnp.int32, (8, 2 * n), 0)
    for j in range(0, n, 2):
        at, low = j // 8, j % 8
        one = bands[at][low : low + 1, :]
        two = bands[at][low + 1 : low + 2, :]
        a, b, c = one[:, j : j + 1], one[:, j + 1 : j + 2], two[:, j + 1 : j + 2]
        scale = 1.0 / (a * c - b * b)
        to_one = (c * scale) * one - (b * scale) * two
        to_two = (a * scale) * two - (b * scale) * one
        for i in range(at, n // 8):
            update = bands[i][:, j : j + 1] * to_one + bands[i][:, j + 1 : j + 2] * to_two
            if i == at:
                update = jnp.where(line > low + 1, update, 0.0)
            bands[i] = bands[i] - update
    table = jnp.concatenate(bands, 0)
    left, right = table[:, :n], table[:, n:]
    pivots = jnp.sum(jnp.where(row == col, left, 0.0), 1, keepdims=True)
    beside = jnp.sum(jnp.where(row + 1 == col, left, 0.0), 1, keepdims=True)
    odd = row % 2 == 1
    ratio = beside / pivots
    above = pltpu.roll(jnp.broadcast_to(ratio, (n, n)), 1, 0)
    right = jnp.where(odd, right - above * pltpu.roll(right, 1, 0), right)
    cut = pltpu.roll(jnp.broadcast_to(ratio * beside, (n, n)), 1, 0)
    return right / jnp.sqrt(jnp.where(odd, pivots - cut, pivots))


def last_kernel(total_nodes, filtered_ref, *refs):
    parts, (ritz_ref, rayleigh_ref) = refs[:-2], refs[-2:]
    n = filtered_ref.shape[0]
    half = n // 2
    sums = tree_sum([part[...] for part in parts]) * (1.0 / total_nodes)
    packed = jnp.concatenate([sums[:half, :n], sums[:half, n:]], 0)
    row, col = square_index(n)
    upper = jnp.where(col > row, packed, 0.0)
    gram = jnp.where(col >= row, packed, 0.0) + upper.T
    lower = jnp.where(col < row, packed, 0.0)
    diagonal = jnp.broadcast_to(sums[half : half + 1, :n], (n, n))
    projected = lower + lower.T + jnp.where(row == col, diagonal, 0.0)
    inverse = inverse_factor(gram)

    def dot(a, b, dims):
        return lax.dot_general(a, b, dims, precision=HIGHEST, preferred_element_type=F32)

    half_way = dot(inverse, projected, NN)
    rayleigh_ref[...] = dot(half_way, inverse, NT)
    turned = dot(inverse, half_way, NT)
    ritz_ref[...] = dot(dot(turned, inverse, NN), filtered_ref[...], NN)


def tree_sum(parts):
    while len(parts) > 1:
        parts = [a + b for a, b in zip(parts[::2], parts[1::2])]
    return parts[0]


def local(tiles, tile_rows, tile_cols, start):
    tiles, tile_rows, tile_cols = tiles[0, 0], tile_rows[0, 0], tile_cols[0, 0]
    width = tiles.shape[-1]
    vectors_n, own_nodes = start.shape
    rows_n, cols_n = lax.axis_size("row"), lax.axis_size("col")
    chips_n = cols_n // 2
    total_nodes = own_nodes * rows_n * cols_n
    group = own_nodes // width
    spread = (vectors_n, tiles.shape[0] * width)

    rounded_shape = jax.ShapeDtypeStruct((group, vectors_n, width), BF16)
    vector_shape = jax.ShapeDtypeStruct((vectors_n, own_nodes), F32)
    degree_shape = jax.ShapeDtypeStruct((group, width), F32)

    col_apart = (tile_cols // group) ^ lax.axis_index("row")
    row_apart = (tile_rows // group) ^ lax.axis_index("col")
    row_halves = row_apart % 2 * chips_n + row_apart // 2
    table = jnp.stack([col_apart, row_apart, row_halves]) * group
    table = (table + jnp.stack([tile_cols, tile_rows, tile_rows]) % group).astype(jnp.int32)

    col_offsets, d = [0], rows_n // 2
    while d:
        col_offsets += [offset ^ d for offset in col_offsets]
        d //= 2
    row_offsets = [2 * d + core for core in range(2) for d in range(chips_n)]
    offsets = (col_offsets, row_offsets)

    def gather(rounded):
        held, d = [rounded], rows_n // 2
        while d:
            near = trade(rounded, "row", d)
            if len(held) > 1:
                near, *rest = lax.optimization_barrier((near, *held[1:]))
                held = [rounded, *rest]
            held += [near, *(trade(part, "row", d) for part in held[1:])]
            d //= 2
        chips = [rounded, *exchange([rounded] * (chips_n - 1), "col", 2)]
        return held, chips + [trade(chip, "col", 1) for chip in chips]

    def apply(rounded, degree=()):
        kept, swap, col_own, col_send = products(tiles, table, *gather(rounded), offsets, degree)
        col_got = exchange(col_send, "row")
        row_own, *row_send = merge(kept, trade(swap, "col", 1), degree)
        if degree:
            own_degree, *row_send = row_send
        row_got = exchange(row_send, "col", 2)
        sums = [row_own, col_own, *row_got, *col_got]
        return [own_degree, degree[1], *sums] if degree else sums

    rounded = call(round_kernel, rounded_shape, [], 16, [start])
    degree = call(
        degree_kernel,
        [jax.ShapeDtypeStruct((n * group, width), F32) for n in (cols_n, rows_n)],
        [],
        16,
        [table, tiles],
        4 * tiles.size * DEGREE_ROWS,
        1,
    )
    first, rounded, degree = call(
        functools.partial(first_kernel, chips_n),
        [vector_shape, rounded_shape, degree_shape],
        [],
        24,
        [start, *apply(rounded, tuple(degree))],
    )
    filtered, rounded, gram = call(
        functools.partial(filter_kernel, chips_n),
        [vector_shape, rounded_shape, jax.ShapeDtypeStruct((vectors_n, 2 * vectors_n), F32)],
        [pltpu.VMEM((2 * vectors_n, own_nodes), F32)],
        24,
        [start, first, degree, *apply(rounded)],
    )
    col_parts, row_parts = gather(rounded)
    sums = call(
        functools.partial(form_kernel, offsets),
        jax.ShapeDtypeStruct((vectors_n // 2 + 8, 2 * vectors_n), F32),
        [
            pltpu.VMEM((rows_n * group, vectors_n, width), BF16),
            pltpu.VMEM((cols_n * group, vectors_n, width), BF16),
            pltpu.VMEM(spread, BF16),
            pltpu.VMEM(spread, BF16),
        ],
        24,
        [table, tiles, gram, *col_parts, *row_parts],
        4 * tiles.size * vectors_n,
        1,
    )
    sums = sums + trade(sums, "col", 1)
    sums = tree_sum([sums, *exchange([sums] * (chips_n - 1), "col", 2)])
    return call(
        functools.partial(last_kernel, total_nodes),
        [vector_shape, jax.ShapeDtypeStruct((vectors_n, vectors_n), F32)],
        [],
        24,
        [filtered, sums, *exchange([sums] * (rows_n - 1), "row")],
    )


def solution(mesh):
    placed = (
        P("row", "col", None, None, None),
        P("row", "col", None),
        P("row", "col", None),
        P(None, ("row", "col")),
    )
    return jax.shard_map(
        local, mesh=mesh, in_specs=placed, out_specs=(P(None, ("row", "col")), P()), check_vma=False
    )
```

time: 113 us -> 116 us (1.027)
  starting transfers between devices: 52.5 us -> 55.8 us
  Pallas kernels: 14.7 us -> 17.5 us
  waiting for transfers between devices: 41.3 us -> 38.8 us
    ppermute x48 -> x51, starting transfers between devices: 52.5 us -> 55.8 us  [trade(): return lax.ppermute(part, axis, [(i, i ^ d) for i in range(n)])]
    pallas_call x9 -> x10, Pallas kernels: 14.7 us -> 17.5 us  [call(): pl.pallas_call(kernel, out_shape=out_shape, in_specs=[SMEM] * smem + [VME...]
    ppermute x48 -> x51, waiting for transfers between devices: 41.3 us -> 38.8 us  [trade(): return lax.ppermute(part, axis, [(i, i ^ d) for i in range(n)])]
    unnamed x16 -> x12, local copies, waits for them, and re-layouts: 3.5 us -> 2.83 us
  transfers between devices with their start and end apart: 48 -> 51, of which waited for: 30 -> 27; matrix products, arithmetic and copies ran while one was open for 0% -> 0% of each run, Pallas kernels for 0% -> 2%
where the time goes in v7:
time: 116 us
  starting transfers between devices  55.8 us (48%)
  waiting for transfers between devices  38.8 us (33%)
  Pallas kernels  17.5 us (15%)
  local copies, waits for them, and re-layouts  2.83 us (2%)
    ppermute x51, starting transfers between devices, trade(): return lax.ppermute(part, axis, [(i, i ^ d) for i in range(n)])  55.8 us
    ppermute x51, waiting for transfers between devices, trade(): return lax.ppermute(part, axis, [(i, i ^ d) for i in range(n)])  38.8 us
    pallas_call x10, Pallas kernels, call(): pl.pallas_call(kernel, out_shape=out_shape, in_specs=[SMEM] * smem + [VME...  17.5 us
    unnamed x12, local copies, waits for them, and re-layouts  2.83 us
  transfers between devices with their start and end apart: 51, of which 27 were waited for; matrix products, arithmetic and copies ran while one was open for 0% of the time, Pallas kernels for 2%

profile of v7, /device:TPU:0, one launch (start us, length us, event | category | flops | bytes accessed | tf_op | source)
XLA Modules:
  0.0 115.9 jit_solution(8058579765886163254)
XLA Ops:
  0.6 0.9 copy-done.2
  1.6 4.0 %collective-permute-start.5 = (bf16[8,64,128]{2,1,0:T(8,128)(2,1)S(1)}, bf16[8,64,128]{2,1,0:T(8,128)(2,1)S(1)}, u32[]{:S(2)}, u32[]{:S(2)}) collective-permute-start(bf16[8,64,128]{2,1,0:T(8,128)(2,1)S(1)} %shard_map.59.refs_0_.refs_4_), channel_id=1, source_target_pairs={{0,6},{1,7},{2,4},{3,5},{4,2},{5,3},{6,0},{7,1},{8,14},{9,15},{10,... | collective-permute-start | bytes 393224 | tf_op jit(solution)/shard_map/ppermute | solution.py:37
  6.2 3.0 %collective-permute-start.1 = (bf16[8,64,128]{2,1,0:T(8,128)(2,1)S(1)}, bf16[8,64,128]{2,1,0:T(8,128)(2,1)S(1)}, u32[]{:S(2)}, u32[]{:S(2)}) collective-permute-start(bf16[8,64,128]{2,1,0:T(8,128)(2,1)S(1)} %shard_map.59.refs_0_.refs_4_), channel_id=1, source_target_pairs={{0,16},{8,24},{16,0},{24,8},{1,17},{9,25},{17,1},{25,9},{2,18},{10... | collective-permute-start | bytes 393224 | tf_op jit(solution)/shard_map/ppermute | solution.py:37
  9.2 1.6 %collective-permute-start = (bf16[8,64,128]{2,1,0:T(8,128)(2,1)S(1)}, bf16[8,64,128]{2,1,0:T(8,128)(2,1)S(1)}, u32[]{:S(2)}, u32[]{:S(2)}) collective-permute-start(bf16[8,64,128]{2,1,0:T(8,128)(2,1)S(1)} %shard_map.59.refs_0_.refs_4_), channel_id=1, source_target_pairs={{0,8},{8,0},{16,24},{24,16},{1,9},{9,1},{17,25},{25,17},{2,10},{10... | collective-permute-start | bytes 393224 | tf_op jit(solution)/shard_map/ppermute | solution.py:37
  11.4 3.3 %collective-permute-done.1.refs_1_ = bf16[8,64,128]{2,1,0:T(8,128)(2,1)S(1)} collective-permute-done((bf16[8,64,128]{2,1,0:T(8,128)(2,1)S(1)}, bf16[8,64,128]{2,1,0:T(8,128)(2,1)S(1)}, u32[]{:S(2)}, u32[]{:S(2)}) %collective-permute-start.1) | collective-permute-done | bytes 131104 | tf_op jit(solution)/shard_map/ppermute | solution.py:37
  15.0 1.4 %collective-permute-start.2 = (bf16[8,64,128]{2,1,0:T(8,128)(2,1)S(1)}, bf16[8,64,128]{2,1,0:T(8,128)(2,1)S(1)}, u32[]{:S(2)}, u32[]{:S(2)}) collective-permute-start(bf16[8,64,128]{2,1,0:T(8,128)(2,1)S(1)} %collective-permute-done.1.refs_1_), channel_id=1, source_target_pairs={{0,8},{8,0},{16,24},{24,16},{1,9},{9,1},{17,25},{25,17},{2,10},{10... | collective-permute-start | bytes 393224 | tf_op jit(solution)/shard_map/ppermute | solution.py:37
  17.0 1.2 %copy-done = bf16[1,1,32,128,128]{4,3,2,1,0:T(8,128)(2,1)S(1)} copy-done((bf16[1,1,32,128,128]{4,3,2,1,0:T(8,128)(2,1)S(1)}, bf16[1,1,32,128,128]{4,3,2,1,0:T(8,128)(2,1)}, u32[]{:S(2)}) %copy-start) | copy-done | bytes 1048600
  18.3 1.5 %shard_map.60 = (f32[64,128]{1,0:T(8,128)S(1)}, f32[32,128]{1,0:T(8,128)S(1)}) custom-call(s32[3,32]{1,0:T(4,128)S(1)} %fusion.1.table, bf16[32,128,128]{2,1,0:T(8,128)(2,1)S(1)} %bitcast.6), custom_call_target="tpu_custom_call" | custom-call | flops 33554432 | bytes 1048960 | tf_op jit(solution)/shard_map/pallas_call | solution.py:24
  20.7 1.9 %shard_map.61 = (f32[4,8,64,128]{3,2,1,0:T(8,128)S(1)}, bf16[4,528,128]{2,1,0:T(8,128)(2,1)S(1)}, f32[8,64,128]{2,1,0:T(8,128)S(1)}, bf16[528,128]{1,0:T(8,128)(...) custom-call(s32[3,32]{1,0:T(4,128)S(1)} %fusion.1.table, bf16[32,128,128]{2,1,0:T(8,128)(2,1)S(1)} %bitcast.7, ...), custom_call_target="tpu_custom_call" | custom-call | flops 134217728 | bytes 2670976 | tf_op jit(solution)/shard_map/pallas_call | solution.py:24
  23.4 3.3 %collective-permute-start.15 = (bf16[528,128]{1,0:T(8,128)(2,1)S(1)}, bf16[528,128]{1,0:T(8,128)(2,1)S(1)}, u32[]{:S(2)}, u32[]{:S(2)}) collective-permute-start(bf16[528,128]{1,0:T(8,128)(2,1)S(1)} %get-tuple-element.50), channel_id=1, source_target_pairs={{0,16},{8,24},{16,0},{24,8},{1,17},{9,25},{17,1},{25,9},{2,18},{10... | collective-permute-start | bytes 405512 | tf_op jit(solution)/shard_map/ppermute | solution.py:37
  27.2 1.6 %collective-permute-start.11 = (bf16[528,128]{1,0:T(8,128)(2,1)S(1)}, bf16[528,128]{1,0:T(8,128)(2,1)S(1)}, u32[]{:S(2)}, u32[]{:S(2)}) collective-permute-start(bf16[528,128]{1,0:T(8,128)(2,1)S(1)} %get-tuple-element.46), channel_id=1, source_target_pairs={{0,2},{1,3},{2,0},{3,1},{4,6},{5,7},{6,4},{7,5},{8,10},{9,11},{10,... | collective-permute-start | bytes 405512 | tf_op jit(solution)/shard_map/ppermute | solution.py:37
  28.8 1.5 %collective-permute-start.12 = (bf16[528,128]{1,0:T(8,128)(2,1)S(1)}, bf16[528,128]{1,0:T(8,128)(2,1)S(1)}, u32[]{:S(2)}, u32[]{:S(2)}) collective-permute-start(bf16[528,128]{1,0:T(8,128)(2,1)S(1)} %get-tuple-element.47), channel_id=1, source_target_pairs={{0,4},{1,5},{2,6},{3,7},{4,0},{5,1},{6,2},{7,3},{8,12},{9,13},{10,... | collective-permute-start | bytes 405512 | tf_op jit(solution)/shard_map/ppermute | solution.py:37
  30.4 0.9 collective-permute-done.14.refs_3_
  31.2 2.5 %collective-permute-start.13 = (bf16[528,128]{1,0:T(8,128)(2,1)S(1)}, bf16[528,128]{1,0:T(8,128)(2,1)S(1)}, u32[]{:S(2)}, u32[]{:S(2)}) collective-permute-start(bf16[528,128]{1,0:T(8,128)(2,1)S(1)} %get-tuple-element.48), channel_id=1, source_target_pairs={{0,6},{1,7},{2,4},{3,5},{4,2},{5,3},{6,0},{7,1},{8,14},{9,15},{10,... | collective-permute-start | bytes 405512 | tf_op jit(solution)/shard_map/ppermute | solution.py:37
  33.7 3.2 %collective-permute-done.15.refs_4_ = bf16[528,128]{1,0:T(8,128)(2,1)S(1)} collective-permute-done((bf16[528,128]{1,0:T(8,128)(2,1)S(1)}, bf16[528,128]{1,0:T(8,128)(2,1)S(1)}, u32[]{:S(2)}, u32[]{:S(2)}) %collective-permute-start.15) | collective-permute-done | bytes 135200 | tf_op jit(solution)/shard_map/ppermute | solution.py:37
  37.4 3.7 %collective-permute-start.18 = (bf16[8,64,128]{2,1,0:T(8,128)(2,1)S(1)}, bf16[8,64,128]{2,1,0:T(8,128)(2,1)S(1)}, u32[]{:S(2)}, u32[]{:S(2)}) collective-permute-start(bf16[8,64,128]{2,1,0:T(8,128)(2,1)S(1)} %get-tuple-element.54.refs_0_.refs_4_), channel_id=1, source_target_pairs={{0,16},{8,24},{16,0},{24,8},{1,17},{9,25},{17,1},{25,9},{2,18},{10... | collective-permute-start | bytes 393224 | tf_op jit(solution)/shard_map/ppermute | solution.py:37
  41.1 2.4 %collective-permute-start.22 = (bf16[8,64,128]{2,1,0:T(8,128)(2,1)S(1)}, bf16[8,64,128]{2,1,0:T(8,128)(2,1)S(1)}, u32[]{:S(2)}, u32[]{:S(2)}) collective-permute-start(bf16[8,64,128]{2,1,0:T(8,128)(2,1)S(1)} %get-tuple-element.54.refs_0_.refs_4_), channel_id=1, source_target_pairs={{0,6},{1,7},{2,4},{3,5},{4,2},{5,3},{6,0},{7,1},{8,14},{9,15},{10,... | collective-permute-start | bytes 393224 | tf_op jit(solution)/shard_map/ppermute | solution.py:37
  44.6 2.3 %collective-permute-done.18.refs_1_ = bf16[8,64,128]{2,1,0:T(8,128)(2,1)S(1)} collective-permute-done((bf16[8,64,128]{2,1,0:T(8,128)(2,1)S(1)}, bf16[8,64,128]{2,1,0:T(8,128)(2,1)S(1)}, u32[]{:S(2)}, u32[]{:S(2)}) %collective-permute-start.18) | collective-permute-done | bytes 131104 | tf_op jit(solution)/shard_map/ppermute | solution.py:37
  47.9 1.4 %collective-permute-done.21.refs_6_ = bf16[8,64,128]{2,1,0:T(8,128)(2,1)S(1)} collective-permute-done((bf16[8,64,128]{2,1,0:T(8,128)(2,1)S(1)}, bf16[8,64,128]{2,1,0:T(8,128)(2,1)S(1)}, u32[]{:S(2)}, u32[]{:S(2)}) %collective-permute-start.21) | collective-permute-done | bytes 131104 | tf_op jit(solution)/shard_map/ppermute | solution.py:37
  49.8 1.8 %collective-permute-start.19 = (bf16[8,64,128]{2,1,0:T(8,128)(2,1)S(1)}, bf16[8,64,128]{2,1,0:T(8,128)(2,1)S(1)}, u32[]{:S(2)}, u32[]{:S(2)}) collective-permute-start(bf16[8,64,128]{2,1,0:T(8,128)(2,1)S(1)} %collective-permute-done.18.refs_1_), channel_id=1, source_target_pairs={{0,8},{8,0},{16,24},{24,16},{1,9},{9,1},{17,25},{25,17},{2,10},{10... | collective-permute-start | bytes 393224 | tf_op jit(solution)/shard_map/ppermute | solution.py:37
  51.6 3.7 %collective-permute-done.19.refs_3_ = bf16[8,64,128]{2,1,0:T(8,128)(2,1)S(1)} collective-permute-done((bf16[8,64,128]{2,1,0:T(8,128)(2,1)S(1)}, bf16[8,64,128]{2,1,0:T(8,128)(2,1)S(1)}, u32[]{:S(2)}, u32[]{:S(2)}) %collective-permute-start.19) | collective-permute-done | bytes 131104 | tf_op jit(solution)/shard_map/ppermute | solution.py:37
  55.3 1.9 %shard_map.64 = (f32[4,8,64,128]{3,2,1,0:T(8,128)S(1)}, bf16[4,512,128]{2,1,0:T(8,128)(2,1)S(1)}, f32[8,64,128]{2,1,0:T(8,128)S(1)}, bf16[512,128]{1,0:T(8,128)(...) custom-call(s32[3,32]{1,0:T(4,128)S(1)} %fusion.1.table, bf16[32,128,128]{2,1,0:T(8,128)(2,1)S(1)} %bitcast.8, ...), custom_call_target="tpu_custom_call" | custom-call | flops 134217728 | bytes 2621824 | tf_op jit(solution)/shard_map/pallas_call | solution.py:24
  57.3 1.8 %collective-permute-start.31 = (bf16[512,128]{1,0:T(8,128)(2,1)S(1)}, bf16[512,128]{1,0:T(8,128)(2,1)S(1)}, u32[]{:S(2)}, u32[]{:S(2)}) collective-permute-start(bf16[512,128]{1,0:T(8,128)(2,1)S(1)} %get-tuple-element.64), channel_id=1, source_target_pairs={{0,8},{8,0},{16,24},{24,16},{1,9},{9,1},{17,25},{25,17},{2,10},{10... | collective-permute-start | bytes 393224 | tf_op jit(solution)/shard_map/ppermute | solution.py:37
  59.7 2.0 %collective-permute-start.33 = (bf16[512,128]{1,0:T(8,128)(2,1)S(1)}, bf16[512,128]{1,0:T(8,128)(2,1)S(1)}, u32[]{:S(2)}, u32[]{:S(2)}) collective-permute-start(bf16[512,128]{1,0:T(8,128)(2,1)S(1)} %get-tuple-element.66), channel_id=1, source_target_pairs={{0,24},{8,16},{16,8},{24,0},{1,25},{9,17},{17,9},{25,1},{2,26},{10... | collective-permute-start | bytes 393224 | tf_op jit(solution)/shard_map/ppermute | solution.py:37
  61.8 1.6 %collective-permute-start.28 = (bf16[512,128]{1,0:T(8,128)(2,1)S(1)}, bf16[512,128]{1,0:T(8,128)(2,1)S(1)}, u32[]{:S(2)}, u32[]{:S(2)}) collective-permute-start(bf16[512,128]{1,0:T(8,128)(2,1)S(1)} %get-tuple-element.61), channel_id=1, source_target_pairs={{0,2},{1,3},{2,0},{3,1},{4,6},{5,7},{6,4},{7,5},{8,10},{9,11},{10,... | collective-permute-start | bytes 393224 | tf_op jit(solution)/shard_map/ppermute | solution.py:37
  64.1 0.9 collective-permute-done.31.refs_3_
  65.0 1.7 %collective-permute-start.30 = (bf16[512,128]{1,0:T(8,128)(2,1)S(1)}, bf16[512,128]{1,0:T(8,128)(2,1)S(1)}, u32[]{:S(2)}, u32[]{:S(2)}) collective-permute-start(bf16[512,128]{1,0:T(8,128)(2,1)S(1)} %get-tuple-element.63), channel_id=1, source_target_pairs={{0,6},{1,7},{2,4},{3,5},{4,2},{5,3},{6,0},{7,1},{8,14},{9,15},{10,... | collective-permute-start | bytes 393224 | tf_op jit(solution)/shard_map/ppermute | solution.py:37
  66.7 5.3 %collective-permute-done.32.refs_4_ = bf16[512,128]{1,0:T(8,128)(2,1)S(1)} collective-permute-done((bf16[512,128]{1,0:T(8,128)(2,1)S(1)}, bf16[512,128]{1,0:T(8,128)(2,1)S(1)}, u32[]{:S(2)}, u32[]{:S(2)}) %collective-permute-start.32) | collective-permute-done | bytes 131104 | tf_op jit(solution)/shard_map/ppermute | solution.py:37
  72.8 3.0 %collective-permute-start.35 = (bf16[8,64,128]{2,1,0:T(8,128)(2,1)S(1)}, bf16[8,64,128]{2,1,0:T(8,128)(2,1)S(1)}, u32[]{:S(2)}, u32[]{:S(2)}) collective-permute-start(bf16[8,64,128]{2,1,0:T(8,128)(2,1)S(1)} %get-tuple-element.69.refs_0_.refs_4_), channel_id=1, source_target_pairs={{0,16},{8,24},{16,0},{24,8},{1,17},{9,25},{17,1},{25,9},{2,18},{10... | collective-permute-start | bytes 393224 | tf_op jit(solution)/shard_map/ppermute | solution.py:37
  75.7 1.7 %collective-permute-start.39 = (bf16[8,64,128]{2,1,0:T(8,128)(2,1)S(1)}, bf16[8,64,128]{2,1,0:T(8,128)(2,1)S(1)}, u32[]{:S(2)}, u32[]{:S(2)}) collective-permute-start(bf16[8,64,128]{2,1,0:T(8,128)(2,1)S(1)} %get-tuple-element.69.refs_0_.refs_4_), channel_id=1, source_target_pairs={{0,6},{1,7},{2,4},{3,5},{4,2},{5,3},{6,0},{7,1},{8,14},{9,15},{10,... | collective-permute-start | bytes 393224 | tf_op jit(solution)/shard_map/ppermute | solution.py:37
  77.4 1.3 %collective-permute-start.38 = (bf16[8,64,128]{2,1,0:T(8,128)(2,1)S(1)}, bf16[8,64,128]{2,1,0:T(8,128)(2,1)S(1)}, u32[]{:S(2)}, u32[]{:S(2)}) collective-permute-start(bf16[8,64,128]{2,1,0:T(8,128)(2,1)S(1)} %get-tuple-element.69.refs_0_.refs_4_), channel_id=1, source_target_pairs={{0,4},{1,5},{2,6},{3,7},{4,0},{5,1},{6,2},{7,3},{8,12},{9,13},{10,... | collective-permute-start | bytes 393224 | tf_op jit(solution)/shard_map/ppermute | solution.py:37
  79.2 1.7 %collective-permute-done.35.refs_1_ = bf16[8,64,128]{2,1,0:T(8,128)(2,1)S(1)} collective-permute-done((bf16[8,64,128]{2,1,0:T(8,128)(2,1)S(1)}, bf16[8,64,128]{2,1,0:T(8,128)(2,1)S(1)}, u32[]{:S(2)}, u32[]{:S(2)}) %collective-permute-start.35) | collective-permute-done | bytes 131104 | tf_op jit(solution)/shard_map/ppermute | solution.py:37
  81.5 1.2 %collective-permute-done.39.refs_7_ = bf16[8,64,128]{2,1,0:T(8,128)(2,1)S(1)} collective-permute-done((bf16[8,64,128]{2,1,0:T(8,128)(2,1)S(1)}, bf16[8,64,128]{2,1,0:T(8,128)(2,1)S(1)}, u32[]{:S(2)}, u32[]{:S(2)}) %collective-permute-start.39) | collective-permute-done | bytes 131104 | tf_op jit(solution)/shard_map/ppermute | solution.py:37
  82.8 1.1 collective-permute-done.38.refs_6_
  84.4 1.7 %collective-permute-start.36 = (bf16[8,64,128]{2,1,0:T(8,128)(2,1)S(1)}, bf16[8,64,128]{2,1,0:T(8,128)(2,1)S(1)}, u32[]{:S(2)}, u32[]{:S(2)}) collective-permute-start(bf16[8,64,128]{2,1,0:T(8,128)(2,1)S(1)} %collective-permute-done.35.refs_1_), channel_id=1, source_target_pairs={{0,8},{8,0},{16,24},{24,16},{1,9},{9,1},{17,25},{25,17},{2,10},{10... | collective-permute-start | bytes 393224 | tf_op jit(solution)/shard_map/ppermute | solution.py:37
  86.2 3.7 %collective-permute-done.36.refs_3_ = bf16[8,64,128]{2,1,0:T(8,128)(2,1)S(1)} collective-permute-done((bf16[8,64,128]{2,1,0:T(8,128)(2,1)S(1)}, bf16[8,64,128]{2,1,0:T(8,128)(2,1)S(1)}, u32[]{:S(2)}, u32[]{:S(2)}) %collective-permute-start.36) | collective-permute-done | bytes 131104 | tf_op jit(solution)/shard_map/ppermute | solution.py:37
  89.9 2.0 %shard_map.67 = f32[40,128]{1,0:T(8,128)S(1)} custom-call(s32[3,32]{1,0:T(4,128)S(1)} %fusion.1.table, bf16[32,128,128]{2,1,0:T(8,128)(2,1)S(1)} %bitcast.9, f32[64,128]{1,0:T(8,128)S(1)} %get-tuple-element.68.gram_ref, bf16[8,64,128]{2,1,0:T(8,128)(2,1)S(1)} %get-tuple-element.69.refs_0_.refs_4_, bf16[8,64,128]{2,1,0:T(8,128)(2,1)S(1)} %collective-permute-done.35.refs_1_, ...), custom_call_target="tpu_custom_call" | custom-call | flops 134217728 | bytes 2654592 | tf_op jit(solution)/shard_map/pallas_call | solution.py:24
  92.0 1.2 %collective-permute-done.44 = f32[40,128]{1,0:T(8,128)S(1)} collective-permute-done((f32[40,128]{1,0:T(8,128)S(1)}, f32[40,128]{1,0:T(8,128)S(1)}, u32[]{:S(2)}, u32[]{:S(2)}) %collective-permute-start.44) | collective-permute-done | bytes 20512 | tf_op jit(solution)/shard_map/ppermute | solution.py:37
  93.2 1.6 %collective-permute-start.47 = (f32[40,128]{1,0:T(8,128)S(1)}, f32[40,128]{1,0:T(8,128)S(1)}, u32[]{:S(2)}, u32[]{:S(2)}) collective-permute-start(f32[40,128]{1,0:T(8,128)S(1)} %add.76), channel_id=1, source_target_pairs={{0,6},{1,7},{2,4},{3,5},{4,2},{5,3},{6,0},{7,1},{8,14},{9,15},{10,... | collective-permute-start | bytes 61448 | tf_op jit(solution)/shard_map/ppermute | solution.py:37
  94.7 1.3 %collective-permute-start.46 = (f32[40,128]{1,0:T(8,128)S(1)}, f32[40,128]{1,0:T(8,128)S(1)}, u32[]{:S(2)}, u32[]{:S(2)}) collective-permute-start(f32[40,128]{1,0:T(8,128)S(1)} %add.76), channel_id=1, source_target_pairs={{0,4},{1,5},{2,6},{3,7},{4,0},{5,1},{6,2},{7,3},{8,12},{9,13},{10,... | collective-permute-start | bytes 61448 | tf_op jit(solution)/shard_map/ppermute | solution.py:37
  96.7 1.2 %collective-permute-done.47 = f32[40,128]{1,0:T(8,128)S(1)} collective-permute-done((f32[40,128]{1,0:T(8,128)S(1)}, f32[40,128]{1,0:T(8,128)S(1)}, u32[]{:S(2)}, u32[]{:S(2)}) %collective-permute-start.47) | collective-permute-done | bytes 20512 | tf_op jit(solution)/shard_map/ppermute | solution.py:37
  98.5 1.3 %collective-permute-done.45 = f32[40,128]{1,0:T(8,128)S(1)} collective-permute-done((f32[40,128]{1,0:T(8,128)S(1)}, f32[40,128]{1,0:T(8,128)S(1)}, u32[]{:S(2)}, u32[]{:S(2)}) %collective-permute-start.45) | collective-permute-done | bytes 20512 | tf_op jit(solution)/shard_map/ppermute | solution.py:37
  99.8 2.1 %collective-permute-start.50 = (f32[40,128]{1,0:T(8,128)S(1)}, f32[40,128]{1,0:T(8,128)S(1)}, u32[]{:S(2)}, u32[]{:S(2)}) collective-permute-start(f32[40,128]{1,0:T(8,128)S(1)} %add_add_fusion.refs_0_), channel_id=1, source_target_pairs={{0,24},{8,16},{16,8},{24,0},{1,25},{9,17},{17,9},{25,1},{2,26},{10... | collective-permute-start | bytes 61448 | tf_op jit(solution)/shard_map/ppermute | solution.py:37
  101.9 1.2 %collective-permute-start.49 = (f32[40,128]{1,0:T(8,128)S(1)}, f32[40,128]{1,0:T(8,128)S(1)}, u32[]{:S(2)}, u32[]{:S(2)}) collective-permute-start(f32[40,128]{1,0:T(8,128)S(1)} %add_add_fusion.refs_0_), channel_id=1, source_target_pairs={{0,16},{8,24},{16,0},{24,8},{1,17},{9,25},{17,1},{25,9},{2,18},{10... | collective-permute-start | bytes 61448 | tf_op jit(solution)/shard_map/ppermute | solution.py:37
  103.1 1.2 %collective-permute-start.48 = (f32[40,128]{1,0:T(8,128)S(1)}, f32[40,128]{1,0:T(8,128)S(1)}, u32[]{:S(2)}, u32[]{:S(2)}) collective-permute-start(f32[40,128]{1,0:T(8,128)S(1)} %add_add_fusion.refs_0_), channel_id=1, source_target_pairs={{0,8},{8,0},{16,24},{24,16},{1,9},{9,1},{17,25},{25,17},{2,10},{10... | collective-permute-start | bytes 61448 | tf_op jit(solution)/shard_map/ppermute | solution.py:37
  104.3 1.2 %collective-permute-done.50.refs_3_ = f32[40,128]{1,0:T(8,128)S(1)} collective-permute-done((f32[40,128]{1,0:T(8,128)S(1)}, f32[40,128]{1,0:T(8,128)S(1)}, u32[]{:S(2)}, u32[]{:S(2)}) %collective-permute-start.50) | collective-permute-done | bytes 20512 | tf_op jit(solution)/shard_map/ppermute | solution.py:37
  105.5 1.1 collective-permute-done.49.refs_2_
  106.9 9.0 %shard_map.68 = (f32[64,1024]{1,0:T(8,128)}, f32[64,64]{1,0:T(8,128)}) custom-call(f32[64,1024]{1,0:T(8,128)S(1)} %get-tuple-element.67.filtered_ref, f32[40,128]{1,0:T(8,128)S(1)} %add_add_fusion.refs_0_, f32[40,128]{1,0:T(8,128)S(1)} %collective-permute-done.48.refs_1_, f32[40,128]{1,0:T(8,128)S(1)} %collective-permute-done.49.refs_2_, ...), custom_call_target="tpu_custom_call" | custom-call | bytes 344064 | tf_op jit(solution)/shard_map/pallas_call | solution.py:24
  (81 shorter events, 13.0 us)
Async XLA Ops:
  1.6 14.8 %collective-permute-start.5 = (bf16[8,64,128]{2,1,0:T(8,128)(2,1)S(1)}, bf16[8,64,128]{2,1,0:T(8,128)(2,1)S(1)}, u32[]{:S(2)}, u32[]{:S(2)}) collective-permute-start(bf16[8,64,128]{2,1,0:T(8,128)(2,1)S(1)} %shard_map.59.refs_0_.refs_4_), channel_id=1, source_target_pairs={{0,6},{1,7},{2,4},{3,5},{4,2},{5,3},{6,0},{7,1},{8,14},{9,15},{10,... | collective-permute-start | bytes 393224 | tf_op jit(solution)/shard_map/ppermute | solution.py:37
  5.6 10.8 %collective-permute-start.4 = (bf16[8,64,128]{2,1,0:T(8,128)(2,1)S(1)}, bf16[8,64,128]{2,1,0:T(8,128)(2,1)S(1)}, u32[]{:S(2)}, u32[]{:S(2)}) collective-permute-start(bf16[8,64,128]{2,1,0:T(8,128)(2,1)S(1)} %shard_map.59.refs_0_.refs_4_), channel_id=1, source_target_pairs={{0,4},{1,5},{2,6},{3,7},{4,0},{5,1},{6,2},{7,3},{8,12},{9,13},{10,... | collective-permute-start | bytes 393224 | tf_op jit(solution)/shard_map/ppermute | solution.py:37
  6.1 10.9 %collective-permute-start.3 = (bf16[8,64,128]{2,1,0:T(8,128)(2,1)S(1)}, bf16[8,64,128]{2,1,0:T(8,128)(2,1)S(1)}, u32[]{:S(2)}, u32[]{:S(2)}) collective-permute-start(bf16[8,64,128]{2,1,0:T(8,128)(2,1)S(1)} %shard_map.59.refs_0_.refs_4_), channel_id=1, source_target_pairs={{0,2},{1,3},{2,0},{3,1},{4,6},{5,7},{6,4},{7,5},{8,10},{9,11},{10,... | collective-permute-start | bytes 393224 | tf_op jit(solution)/shard_map/ppermute | solution.py:37
  6.2 8.6 %collective-permute-start.1 = (bf16[8,64,128]{2,1,0:T(8,128)(2,1)S(1)}, bf16[8,64,128]{2,1,0:T(8,128)(2,1)S(1)}, u32[]{:S(2)}, u32[]{:S(2)}) collective-permute-start(bf16[8,64,128]{2,1,0:T(8,128)(2,1)S(1)} %shard_map.59.refs_0_.refs_4_), channel_id=1, source_target_pairs={{0,16},{8,24},{16,0},{24,8},{1,17},{9,25},{17,1},{25,9},{2,18},{10... | collective-permute-start | bytes 393224 | tf_op jit(solution)/shard_map/ppermute | solution.py:37
  9.2 5.8 %collective-permute-start = (bf16[8,64,128]{2,1,0:T(8,128)(2,1)S(1)}, bf16[8,64,128]{2,1,0:T(8,128)(2,1)S(1)}, u32[]{:S(2)}, u32[]{:S(2)}) collective-permute-start(bf16[8,64,128]{2,1,0:T(8,128)(2,1)S(1)} %shard_map.59.refs_0_.refs_4_), channel_id=1, source_target_pairs={{0,8},{8,0},{16,24},{24,16},{1,9},{9,1},{17,25},{25,17},{2,10},{10... | collective-permute-start | bytes 393224 | tf_op jit(solution)/shard_map/ppermute | solution.py:37
  14.8 5.0 %collective-permute-start.6 = (bf16[8,64,128]{2,1,0:T(8,128)(2,1)S(1)}, bf16[8,64,128]{2,1,0:T(8,128)(2,1)S(1)}, u32[]{:S(2)}, u32[]{:S(2)}) collective-permute-start(bf16[8,64,128]{2,1,0:T(8,128)(2,1)S(1)} %shard_map.59.refs_0_.refs_4_), channel_id=1, source_target_pairs={{0,1},{1,0},{2,3},{3,2},{4,5},{5,4},{6,7},{7,6},{8,9},{9,8},{10,11... | collective-permute-start | bytes 393224 | tf_op jit(solution)/shard_map/ppermute | solution.py:37
  15.0 5.7 %collective-permute-start.2 = (bf16[8,64,128]{2,1,0:T(8,128)(2,1)S(1)}, bf16[8,64,128]{2,1,0:T(8,128)(2,1)S(1)}, u32[]{:S(2)}, u32[]{:S(2)}) collective-permute-start(bf16[8,64,128]{2,1,0:T(8,128)(2,1)S(1)} %collective-permute-done.1.refs_1_), channel_id=1, source_target_pairs={{0,8},{8,0},{16,24},{24,16},{1,9},{9,1},{17,25},{25,17},{2,10},{10... | collective-permute-start | bytes 393224 | tf_op jit(solution)/shard_map/ppermute | solution.py:37
  16.4 3.4 %collective-permute-start.9 = (bf16[8,64,128]{2,1,0:T(8,128)(2,1)S(1)}, bf16[8,64,128]{2,1,0:T(8,128)(2,1)S(1)}, u32[]{:S(2)}, u32[]{:S(2)}) collective-permute-start(bf16[8,64,128]{2,1,0:T(8,128)(2,1)S(1)} %collective-permute-done.5.refs_7_), channel_id=1, source_target_pairs={{0,1},{1,0},{2,3},{3,2},{4,5},{5,4},{6,7},{7,6},{8,9},{9,8},{10,11... | collective-permute-start | bytes 393224 | tf_op jit(solution)/shard_map/ppermute | solution.py:37
  16.4 3.4 %collective-permute-start.8 = (bf16[8,64,128]{2,1,0:T(8,128)(2,1)S(1)}, bf16[8,64,128]{2,1,0:T(8,128)(2,1)S(1)}, u32[]{:S(2)}, u32[]{:S(2)}) collective-permute-start(bf16[8,64,128]{2,1,0:T(8,128)(2,1)S(1)} %collective-permute-done.4.refs_6_), channel_id=1, source_target_pairs={{0,1},{1,0},{2,3},{3,2},{4,5},{5,4},{6,7},{7,6},{8,9},{9,8},{10,11... | collective-permute-start | bytes 393224 | tf_op jit(solution)/shard_map/ppermute | solution.py:37
  16.9 2.9 %collective-permute-start.7 = (bf16[8,64,128]{2,1,0:T(8,128)(2,1)S(1)}, bf16[8,64,128]{2,1,0:T(8,128)(2,1)S(1)}, u32[]{:S(2)}, u32[]{:S(2)}) collective-permute-start(bf16[8,64,128]{2,1,0:T(8,128)(2,1)S(1)} %collective-permute-done.3.refs_5_), channel_id=1, source_target_pairs={{0,1},{1,0},{2,3},{3,2},{4,5},{5,4},{6,7},{7,6},{8,9},{9,8},{10,11... | collective-permute-start | bytes 393224 | tf_op jit(solution)/shard_map/ppermute | solution.py:37
  22.6 4.5 %collective-permute-start.10 = (bf16[4,528,128]{2,1,0:T(8,128)(2,1)S(1)}, bf16[4,528,128]{2,1,0:T(8,128)(2,1)S(1)}, u32[]{:S(2)}, u32[]{:S(2)}) collective-permute-start(bf16[4,528,128]{2,1,0:T(8,128)(2,1)S(1)} %get-tuple-element.42), channel_id=1, source_target_pairs={{0,1},{1,0},{2,3},{3,2},{4,5},{5,4},{6,7},{7,6},{8,9},{9,8},{10,11... | collective-permute-start | bytes 1622024 | tf_op jit(solution)/shard_map/ppermute | solution.py:37
  22.7 8.6 %collective-permute-start.14 = (bf16[528,128]{1,0:T(8,128)(2,1)S(1)}, bf16[528,128]{1,0:T(8,128)(2,1)S(1)}, u32[]{:S(2)}, u32[]{:S(2)}) collective-permute-start(bf16[528,128]{1,0:T(8,128)(2,1)S(1)} %get-tuple-element.49), channel_id=1, source_target_pairs={{0,8},{8,0},{16,24},{24,16},{1,9},{9,1},{17,25},{25,17},{2,10},{10... | collective-permute-start | bytes 405512 | tf_op jit(solution)/shard_map/ppermute | solution.py:37
  23.4 13.5 %collective-permute-start.15 = (bf16[528,128]{1,0:T(8,128)(2,1)S(1)}, bf16[528,128]{1,0:T(8,128)(2,1)S(1)}, u32[]{:S(2)}, u32[]{:S(2)}) collective-permute-start(bf16[528,128]{1,0:T(8,128)(2,1)S(1)} %get-tuple-element.50), channel_id=1, source_target_pairs={{0,16},{8,24},{16,0},{24,8},{1,17},{9,25},{17,1},{25,9},{2,18},{10... | collective-permute-start | bytes 405512 | tf_op jit(solution)/shard_map/ppermute | solution.py:37
  26.7 10.2 %collective-permute-start.16 = (bf16[528,128]{1,0:T(8,128)(2,1)S(1)}, bf16[528,128]{1,0:T(8,128)(2,1)S(1)}, u32[]{:S(2)}, u32[]{:S(2)}) collective-permute-start(bf16[528,128]{1,0:T(8,128)(2,1)S(1)} %get-tuple-element.51), channel_id=1, source_target_pairs={{0,24},{8,16},{16,8},{24,0},{1,25},{9,17},{17,9},{25,1},{2,26},{10... | collective-permute-start | bytes 405512 | tf_op jit(solution)/shard_map/ppermute | solution.py:37
  27.2 9.7 %collective-permute-start.11 = (bf16[528,128]{1,0:T(8,128)(2,1)S(1)}, bf16[528,128]{1,0:T(8,128)(2,1)S(1)}, u32[]{:S(2)}, u32[]{:S(2)}) collective-permute-start(bf16[528,128]{1,0:T(8,128)(2,1)S(1)} %get-tuple-element.46), channel_id=1, source_target_pairs={{0,2},{1,3},{2,0},{3,1},{4,6},{5,7},{6,4},{7,5},{8,10},{9,11},{10,... | collective-permute-start | bytes 405512 | tf_op jit(solution)/shard_map/ppermute | solution.py:37
  28.8 8.1 %collective-permute-start.12 = (bf16[528,128]{1,0:T(8,128)(2,1)S(1)}, bf16[528,128]{1,0:T(8,128)(2,1)S(1)}, u32[]{:S(2)}, u32[]{:S(2)}) collective-permute-start(bf16[528,128]{1,0:T(8,128)(2,1)S(1)} %get-tuple-element.47), channel_id=1, source_target_pairs={{0,4},{1,5},{2,6},{3,7},{4,0},{5,1},{6,2},{7,3},{8,12},{9,13},{10,... | collective-permute-start | bytes 405512 | tf_op jit(solution)/shard_map/ppermute | solution.py:37
  31.2 6.0 %collective-permute-start.13 = (bf16[528,128]{1,0:T(8,128)(2,1)S(1)}, bf16[528,128]{1,0:T(8,128)(2,1)S(1)}, u32[]{:S(2)}, u32[]{:S(2)}) collective-permute-start(bf16[528,128]{1,0:T(8,128)(2,1)S(1)} %get-tuple-element.48), channel_id=1, source_target_pairs={{0,6},{1,7},{2,4},{3,5},{4,2},{5,3},{6,0},{7,1},{8,14},{9,15},{10,... | collective-permute-start | bytes 405512 | tf_op jit(solution)/shard_map/ppermute | solution.py:37
  37.4 9.5 %collective-permute-start.18 = (bf16[8,64,128]{2,1,0:T(8,128)(2,1)S(1)}, bf16[8,64,128]{2,1,0:T(8,128)(2,1)S(1)}, u32[]{:S(2)}, u32[]{:S(2)}) collective-permute-start(bf16[8,64,128]{2,1,0:T(8,128)(2,1)S(1)} %get-tuple-element.54.refs_0_.refs_4_), channel_id=1, source_target_pairs={{0,16},{8,24},{16,0},{24,8},{1,17},{9,25},{17,1},{25,9},{2,18},{10... | collective-permute-start | bytes 393224 | tf_op jit(solution)/shard_map/ppermute | solution.py:37
  41.1 6.1 %collective-permute-start.17 = (bf16[8,64,128]{2,1,0:T(8,128)(2,1)S(1)}, bf16[8,64,128]{2,1,0:T(8,128)(2,1)S(1)}, u32[]{:S(2)}, u32[]{:S(2)}) collective-permute-start(bf16[8,64,128]{2,1,0:T(8,128)(2,1)S(1)} %get-tuple-element.54.refs_0_.refs_4_), channel_id=1, source_target_pairs={{0,8},{8,0},{16,24},{24,16},{1,9},{9,1},{17,25},{25,17},{2,10},{10... | collective-permute-start | bytes 393224 | tf_op jit(solution)/shard_map/ppermute | solution.py:37
  41.1 6.8 %collective-permute-start.22 = (bf16[8,64,128]{2,1,0:T(8,128)(2,1)S(1)}, bf16[8,64,128]{2,1,0:T(8,128)(2,1)S(1)}, u32[]{:S(2)}, u32[]{:S(2)}) collective-permute-start(bf16[8,64,128]{2,1,0:T(8,128)(2,1)S(1)} %get-tuple-element.54.refs_0_.refs_4_), channel_id=1, source_target_pairs={{0,6},{1,7},{2,4},{3,5},{4,2},{5,3},{6,0},{7,1},{8,14},{9,15},{10,... | collective-permute-start | bytes 393224 | tf_op jit(solution)/shard_map/ppermute | solution.py:37
  43.6 5.7 %collective-permute-start.21 = (bf16[8,64,128]{2,1,0:T(8,128)(2,1)S(1)}, bf16[8,64,128]{2,1,0:T(8,128)(2,1)S(1)}, u32[]{:S(2)}, u32[]{:S(2)}) collective-permute-start(bf16[8,64,128]{2,1,0:T(8,128)(2,1)S(1)} %get-tuple-element.54.refs_0_.refs_4_), channel_id=1, source_target_pairs={{0,4},{1,5},{2,6},{3,7},{4,0},{5,1},{6,2},{7,3},{8,12},{9,13},{10,... | collective-permute-start | bytes 393224 | tf_op jit(solution)/shard_map/ppermute | solution.py:37
  44.1 5.3 %collective-permute-start.20 = (bf16[8,64,128]{2,1,0:T(8,128)(2,1)S(1)}, bf16[8,64,128]{2,1,0:T(8,128)(2,1)S(1)}, u32[]{:S(2)}, u32[]{:S(2)}) collective-permute-start(bf16[8,64,128]{2,1,0:T(8,128)(2,1)S(1)} %get-tuple-element.54.refs_0_.refs_4_), channel_id=1, source_target_pairs={{0,2},{1,3},{2,0},{3,1},{4,6},{5,7},{6,4},{7,5},{8,10},{9,11},{10,... | collective-permute-start | bytes 393224 | tf_op jit(solution)/shard_map/ppermute | solution.py:37
  46.9 4.7 %collective-permute-start.23 = (bf16[8,64,128]{2,1,0:T(8,128)(2,1)S(1)}, bf16[8,64,128]{2,1,0:T(8,128)(2,1)S(1)}, u32[]{:S(2)}, u32[]{:S(2)}) collective-permute-start(bf16[8,64,128]{2,1,0:T(8,128)(2,1)S(1)} %get-tuple-element.54.refs_0_.refs_4_), channel_id=1, source_target_pairs={{0,1},{1,0},{2,3},{3,2},{4,5},{5,4},{6,7},{7,6},{8,9},{9,8},{10,11... | collective-permute-start | bytes 393224 | tf_op jit(solution)/shard_map/ppermute | solution.py:37
  47.9 3.7 %collective-permute-start.26 = (bf16[8,64,128]{2,1,0:T(8,128)(2,1)S(1)}, bf16[8,64,128]{2,1,0:T(8,128)(2,1)S(1)}, u32[]{:S(2)}, u32[]{:S(2)}) collective-permute-start(bf16[8,64,128]{2,1,0:T(8,128)(2,1)S(1)} %collective-permute-done.22.refs_7_), channel_id=1, source_target_pairs={{0,1},{1,0},{2,3},{3,2},{4,5},{5,4},{6,7},{7,6},{8,9},{9,8},{10,11... | collective-permute-start | bytes 393224 | tf_op jit(solution)/shard_map/ppermute | solution.py:37
  49.3 2.3 %collective-permute-start.25 = (bf16[8,64,128]{2,1,0:T(8,128)(2,1)S(1)}, bf16[8,64,128]{2,1,0:T(8,128)(2,1)S(1)}, u32[]{:S(2)}, u32[]{:S(2)}) collective-permute-start(bf16[8,64,128]{2,1,0:T(8,128)(2,1)S(1)} %collective-permute-done.21.refs_6_), channel_id=1, source_target_pairs={{0,1},{1,0},{2,3},{3,2},{4,5},{5,4},{6,7},{7,6},{8,9},{9,8},{10,11... | collective-permute-start | bytes 393224 | tf_op jit(solution)/shard_map/ppermute | solution.py:37
  49.8 5.5 %collective-permute-start.19 = (bf16[8,64,128]{2,1,0:T(8,128)(2,1)S(1)}, bf16[8,64,128]{2,1,0:T(8,128)(2,1)S(1)}, u32[]{:S(2)}, u32[]{:S(2)}) collective-permute-start(bf16[8,64,128]{2,1,0:T(8,128)(2,1)S(1)} %collective-permute-done.18.refs_1_), channel_id=1, source_target_pairs={{0,8},{8,0},{16,24},{24,16},{1,9},{9,1},{17,25},{25,17},{2,10},{10... | collective-permute-start | bytes 393224 | tf_op jit(solution)/shard_map/ppermute | solution.py:37
  57.2 4.5 %collective-permute-start.27 = (bf16[4,512,128]{2,1,0:T(8,128)(2,1)S(1)}, bf16[4,512,128]{2,1,0:T(8,128)(2,1)S(1)}, u32[]{:S(2)}, u32[]{:S(2)}) collective-permute-start(bf16[4,512,128]{2,1,0:T(8,128)(2,1)S(1)} %get-tuple-element.58), channel_id=1, source_target_pairs={{0,1},{1,0},{2,3},{3,2},{4,5},{5,4},{6,7},{7,6},{8,9},{9,8},{10,11... | collective-permute-start | bytes 1572872 | tf_op jit(solution)/shard_map/ppermute | solution.py:37
  57.3 7.8 %collective-permute-start.31 = (bf16[512,128]{1,0:T(8,128)(2,1)S(1)}, bf16[512,128]{1,0:T(8,128)(2,1)S(1)}, u32[]{:S(2)}, u32[]{:S(2)}) collective-permute-start(bf16[512,128]{1,0:T(8,128)(2,1)S(1)} %get-tuple-element.64), channel_id=1, source_target_pairs={{0,8},{8,0},{16,24},{24,16},{1,9},{9,1},{17,25},{25,17},{2,10},{10... | collective-permute-start | bytes 393224 | tf_op jit(solution)/shard_map/ppermute | solution.py:37
  59.1 12.9 %collective-permute-start.32 = (bf16[512,128]{1,0:T(8,128)(2,1)S(1)}, bf16[512,128]{1,0:T(8,128)(2,1)S(1)}, u32[]{:S(2)}, u32[]{:S(2)}) collective-permute-start(bf16[512,128]{1,0:T(8,128)(2,1)S(1)} %get-tuple-element.65), channel_id=1, source_target_pairs={{0,16},{8,24},{16,0},{24,8},{1,17},{9,25},{17,1},{25,9},{2,18},{10... | collective-permute-start | bytes 393224 | tf_op jit(solution)/shard_map/ppermute | solution.py:37
  59.7 12.3 %collective-permute-start.33 = (bf16[512,128]{1,0:T(8,128)(2,1)S(1)}, bf16[512,128]{1,0:T(8,128)(2,1)S(1)}, u32[]{:S(2)}, u32[]{:S(2)}) collective-permute-start(bf16[512,128]{1,0:T(8,128)(2,1)S(1)} %get-tuple-element.66), channel_id=1, source_target_pairs={{0,24},{8,16},{16,8},{24,0},{1,25},{9,17},{17,9},{25,1},{2,26},{10... | collective-permute-start | bytes 393224 | tf_op jit(solution)/shard_map/ppermute | solution.py:37
  61.8 10.1 %collective-permute-start.28 = (bf16[512,128]{1,0:T(8,128)(2,1)S(1)}, bf16[512,128]{1,0:T(8,128)(2,1)S(1)}, u32[]{:S(2)}, u32[]{:S(2)}) collective-permute-start(bf16[512,128]{1,0:T(8,128)(2,1)S(1)} %get-tuple-element.61), channel_id=1, source_target_pairs={{0,2},{1,3},{2,0},{3,1},{4,6},{5,7},{6,4},{7,5},{8,10},{9,11},{10,... | collective-permute-start | bytes 393224 | tf_op jit(solution)/shard_map/ppermute | solution.py:37
  63.4 8.6 %collective-permute-start.29 = (bf16[512,128]{1,0:T(8,128)(2,1)S(1)}, bf16[512,128]{1,0:T(8,128)(2,1)S(1)}, u32[]{:S(2)}, u32[]{:S(2)}) collective-permute-start(bf16[512,128]{1,0:T(8,128)(2,1)S(1)} %get-tuple-element.62), channel_id=1, source_target_pairs={{0,4},{1,5},{2,6},{3,7},{4,0},{5,1},{6,2},{7,3},{8,12},{9,13},{10,... | collective-permute-start | bytes 393224 | tf_op jit(solution)/shard_map/ppermute | solution.py:37
  65.0 7.0 %collective-permute-start.30 = (bf16[512,128]{1,0:T(8,128)(2,1)S(1)}, bf16[512,128]{1,0:T(8,128)(2,1)S(1)}, u32[]{:S(2)}, u32[]{:S(2)}) collective-permute-start(bf16[512,128]{1,0:T(8,128)(2,1)S(1)} %get-tuple-element.63), channel_id=1, source_target_pairs={{0,6},{1,7},{2,4},{3,5},{4,2},{5,3},{6,0},{7,1},{8,14},{9,15},{10,... | collective-permute-start | bytes 393224 | tf_op jit(solution)/shard_map/ppermute | solution.py:37
  72.8 8.1 %collective-permute-start.35 = (bf16[8,64,128]{2,1,0:T(8,128)(2,1)S(1)}, bf16[8,64,128]{2,1,0:T(8,128)(2,1)S(1)}, u32[]{:S(2)}, u32[]{:S(2)}) collective-permute-start(bf16[8,64,128]{2,1,0:T(8,128)(2,1)S(1)} %get-tuple-element.69.refs_0_.refs_4_), channel_id=1, source_target_pairs={{0,16},{8,24},{16,0},{24,8},{1,17},{9,25},{17,1},{25,9},{2,18},{10... | collective-permute-start | bytes 393224 | tf_op jit(solution)/shard_map/ppermute | solution.py:37
  75.7 5.8 %collective-permute-start.34 = (bf16[8,64,128]{2,1,0:T(8,128)(2,1)S(1)}, bf16[8,64,128]{2,1,0:T(8,128)(2,1)S(1)}, u32[]{:S(2)}, u32[]{:S(2)}) collective-permute-start(bf16[8,64,128]{2,1,0:T(8,128)(2,1)S(1)} %get-tuple-element.69.refs_0_.refs_4_), channel_id=1, source_target_pairs={{0,8},{8,0},{16,24},{24,16},{1,9},{9,1},{17,25},{25,17},{2,10},{10... | collective-permute-start | bytes 393224 | tf_op jit(solution)/shard_map/ppermute | solution.py:37
  75.7 7.1 %collective-permute-start.39 = (bf16[8,64,128]{2,1,0:T(8,128)(2,1)S(1)}, bf16[8,64,128]{2,1,0:T(8,128)(2,1)S(1)}, u32[]{:S(2)}, u32[]{:S(2)}) collective-permute-start(bf16[8,64,128]{2,1,0:T(8,128)(2,1)S(1)} %get-tuple-element.69.refs_0_.refs_4_), channel_id=1, source_target_pairs={{0,6},{1,7},{2,4},{3,5},{4,2},{5,3},{6,0},{7,1},{8,14},{9,15},{10,... | collective-permute-start | bytes 393224 | tf_op jit(solution)/shard_map/ppermute | solution.py:37
  77.4 6.5 %collective-permute-start.38 = (bf16[8,64,128]{2,1,0:T(8,128)(2,1)S(1)}, bf16[8,64,128]{2,1,0:T(8,128)(2,1)S(1)}, u32[]{:S(2)}, u32[]{:S(2)}) collective-permute-start(bf16[8,64,128]{2,1,0:T(8,128)(2,1)S(1)} %get-tuple-element.69.refs_0_.refs_4_), channel_id=1, source_target_pairs={{0,4},{1,5},{2,6},{3,7},{4,0},{5,1},{6,2},{7,3},{8,12},{9,13},{10,... | collective-permute-start | bytes 393224 | tf_op jit(solution)/shard_map/ppermute | solution.py:37
  78.7 5.3 %collective-permute-start.37 = (bf16[8,64,128]{2,1,0:T(8,128)(2,1)S(1)}, bf16[8,64,128]{2,1,0:T(8,128)(2,1)S(1)}, u32[]{:S(2)}, u32[]{:S(2)}) collective-permute-start(bf16[8,64,128]{2,1,0:T(8,128)(2,1)S(1)} %get-tuple-element.69.refs_0_.refs_4_), channel_id=1, source_target_pairs={{0,2},{1,3},{2,0},{3,1},{4,6},{5,7},{6,4},{7,5},{8,10},{9,11},{10,... | collective-permute-start | bytes 393224 | tf_op jit(solution)/shard_map/ppermute | solution.py:37
  80.9 5.3 %collective-permute-start.40 = (bf16[8,64,128]{2,1,0:T(8,128)(2,1)S(1)}, bf16[8,64,128]{2,1,0:T(8,128)(2,1)S(1)}, u32[]{:S(2)}, u32[]{:S(2)}) collective-permute-start(bf16[8,64,128]{2,1,0:T(8,128)(2,1)S(1)} %get-tuple-element.69.refs_0_.refs_4_), channel_id=1, source_target_pairs={{0,1},{1,0},{2,3},{3,2},{4,5},{5,4},{6,7},{7,6},{8,9},{9,8},{10,11... | collective-permute-start | bytes 393224 | tf_op jit(solution)/shard_map/ppermute | solution.py:37
  82.8 3.4 %collective-permute-start.43 = (bf16[8,64,128]{2,1,0:T(8,128)(2,1)S(1)}, bf16[8,64,128]{2,1,0:T(8,128)(2,1)S(1)}, u32[]{:S(2)}, u32[]{:S(2)}) collective-permute-start(bf16[8,64,128]{2,1,0:T(8,128)(2,1)S(1)} %collective-permute-done.39.refs_7_), channel_id=1, source_target_pairs={{0,1},{1,0},{2,3},{3,2},{4,5},{5,4},{6,7},{7,6},{8,9},{9,8},{10,11... | collective-permute-start | bytes 393224 | tf_op jit(solution)/shard_map/ppermute | solution.py:37
  83.9 2.3 %collective-permute-start.42 = (bf16[8,64,128]{2,1,0:T(8,128)(2,1)S(1)}, bf16[8,64,128]{2,1,0:T(8,128)(2,1)S(1)}, u32[]{:S(2)}, u32[]{:S(2)}) collective-permute-start(bf16[8,64,128]{2,1,0:T(8,128)(2,1)S(1)} %collective-permute-done.38.refs_6_), channel_id=1, source_target_pairs={{0,1},{1,0},{2,3},{3,2},{4,5},{5,4},{6,7},{7,6},{8,9},{9,8},{10,11... | collective-permute-start | bytes 393224 | tf_op jit(solution)/shard_map/ppermute | solution.py:37
  84.4 5.5 %collective-permute-start.36 = (bf16[8,64,128]{2,1,0:T(8,128)(2,1)S(1)}, bf16[8,64,128]{2,1,0:T(8,128)(2,1)S(1)}, u32[]{:S(2)}, u32[]{:S(2)}) collective-permute-start(bf16[8,64,128]{2,1,0:T(8,128)(2,1)S(1)} %collective-permute-done.35.refs_1_), channel_id=1, source_target_pairs={{0,8},{8,0},{16,24},{24,16},{1,9},{9,1},{17,25},{25,17},{2,10},{10... | collective-permute-start | bytes 393224 | tf_op jit(solution)/shard_map/ppermute | solution.py:37
  93.2 4.7 %collective-permute-start.47 = (f32[40,128]{1,0:T(8,128)S(1)}, f32[40,128]{1,0:T(8,128)S(1)}, u32[]{:S(2)}, u32[]{:S(2)}) collective-permute-start(f32[40,128]{1,0:T(8,128)S(1)} %add.76), channel_id=1, source_target_pairs={{0,6},{1,7},{2,4},{3,5},{4,2},{5,3},{6,0},{7,1},{8,14},{9,15},{10,... | collective-permute-start | bytes 61448 | tf_op jit(solution)/shard_map/ppermute | solution.py:37
  94.7 3.8 %collective-permute-start.46 = (f32[40,128]{1,0:T(8,128)S(1)}, f32[40,128]{1,0:T(8,128)S(1)}, u32[]{:S(2)}, u32[]{:S(2)}) collective-permute-start(f32[40,128]{1,0:T(8,128)S(1)} %add.76), channel_id=1, source_target_pairs={{0,4},{1,5},{2,6},{3,7},{4,0},{5,1},{6,2},{7,3},{8,12},{9,13},{10,... | collective-permute-start | bytes 61448 | tf_op jit(solution)/shard_map/ppermute | solution.py:37
  96.0 3.8 %collective-permute-start.45 = (f32[40,128]{1,0:T(8,128)S(1)}, f32[40,128]{1,0:T(8,128)S(1)}, u32[]{:S(2)}, u32[]{:S(2)}) collective-permute-start(f32[40,128]{1,0:T(8,128)S(1)} %add.76), channel_id=1, source_target_pairs={{0,2},{1,3},{2,0},{3,1},{4,6},{5,7},{6,4},{7,5},{8,10},{9,11},{10,... | collective-permute-start | bytes 61448 | tf_op jit(solution)/shard_map/ppermute | solution.py:37
  99.8 5.7 %collective-permute-start.50 = (f32[40,128]{1,0:T(8,128)S(1)}, f32[40,128]{1,0:T(8,128)S(1)}, u32[]{:S(2)}, u32[]{:S(2)}) collective-permute-start(f32[40,128]{1,0:T(8,128)S(1)} %add_add_fusion.refs_0_), channel_id=1, source_target_pairs={{0,24},{8,16},{16,8},{24,0},{1,25},{9,17},{17,9},{25,1},{2,26},{10... | collective-permute-start | bytes 61448 | tf_op jit(solution)/shard_map/ppermute | solution.py:37
  101.9 4.7 %collective-permute-start.49 = (f32[40,128]{1,0:T(8,128)S(1)}, f32[40,128]{1,0:T(8,128)S(1)}, u32[]{:S(2)}, u32[]{:S(2)}) collective-permute-start(f32[40,128]{1,0:T(8,128)S(1)} %add_add_fusion.refs_0_), channel_id=1, source_target_pairs={{0,16},{8,24},{16,0},{24,8},{1,17},{9,25},{17,1},{25,9},{2,18},{10... | collective-permute-start | bytes 61448 | tf_op jit(solution)/shard_map/ppermute | solution.py:37
  103.1 3.8 %collective-permute-start.48 = (f32[40,128]{1,0:T(8,128)S(1)}, f32[40,128]{1,0:T(8,128)S(1)}, u32[]{:S(2)}, u32[]{:S(2)}) collective-permute-start(f32[40,128]{1,0:T(8,128)S(1)} %add_add_fusion.refs_0_), channel_id=1, source_target_pairs={{0,8},{8,0},{16,24},{24,16},{1,9},{9,1},{17,25},{25,17},{2,10},{10... | collective-permute-start | bytes 61448 | tf_op jit(solution)/shard_map/ppermute | solution.py:37
  (9 other events, 26.5 us)

commit v8 on v7

--- a/solution.py
+++ b/solution.py
@@ -61,10 +61,12 @@
     return parts[:group] + parts[group:]
 
 
-def fill(panel, parts, offsets):
-    for part, offset in zip(parts, offsets):
-        group = part.shape[0]
-        panel[offset * group : (offset + 1) * group] = part[...]
+def fill(panel, parts, runs):
+    for part, places in zip(parts, runs):
+        at = 0
+        for place, count in places:
+            panel[place : place + count] = part[at : at + count]
+            at += count
 
 
 def degree_kernel(table, tiles_ref, row_ref, col_ref):
@@ -77,19 +79,18 @@
             ref[pl.ds(place, 1), :] += sums[:1]
 
 
-def product_kernel(offsets, degree, table, tiles_ref, *refs):
-    col_offsets, row_offsets = offsets
-    cols_n, rows_n = len(col_offsets), len(row_offsets)
-    half = rows_n // 2
-    col_parts, refs = refs[:cols_n], refs[cols_n:]
-    row_parts, refs = refs[:rows_n], refs[rows_n:]
+def product_kernel(runs, order, degree, table, tiles_ref, *refs):
+    col_runs, row_runs = runs
+    half = len(row_runs) // 2
+    col_parts, refs = refs[: len(col_runs)], refs[len(col_runs) :]
+    row_parts, refs = refs[: len(row_runs)], refs[len(row_runs) :]
     if degree:
         row_degree, col_degree, *refs = refs
     kept_ref, swap_ref, own_ref, *send_refs = refs[:-4]
     col_panel, row_panel, row_total, col_total = refs[-4:]
     group, vectors_n, width = col_parts[0].shape
-    fill(col_panel, col_parts, col_offsets)
-    fill(row_panel, row_parts, row_offsets)
+    fill(col_panel, col_parts, col_runs)
+    fill(row_panel, row_parts, row_runs)
     row_total[...] = jnp.zeros_like(row_total)
     col_total[...] = jnp.zeros_like(col_total)
     for t in range(tiles_ref.shape[0]):
@@ -104,7 +105,7 @@
         kept_ref[d] = row_total[d * group : (d + 1) * group]
     own_ref[...] = col_total[:group]
     sends = [(row_total, half + d, swap_ref.at[d]) for d in range(half)]
-    sends += [(col_total, d, send) for d, send in enumerate(send_refs, 1)]
+    sends += [(col_total, d, send) for d, send in zip(order, send_refs)]
     for total, d, send in sends:
         for k in range(group):
             send[k * vectors_n : (k + 1) * vectors_n, :] = total[d * group + k].astype(BF16)
@@ -113,9 +114,9 @@
             send[group * vectors_n :, :] = split_degree(sums[d * group : (d + 1) * group, :])
 
 
-def products(tiles, table, col_parts, row_parts, offsets, degree):
+def products(tiles, table, col_parts, row_parts, runs, order, degree):
     group, vectors_n, width = col_parts[0].shape
-    rows_n, half = len(offsets[0]), len(offsets[1]) // 2
+    rows_n, half = len(order) + 1, len(row_parts) // 2
     rows = group * vectors_n + (2 * group if degree else 0)
     out_shape = [
         jax.ShapeDtypeStruct((half, group, vectors_n, width), F32),
@@ -129,7 +130,7 @@
         pltpu.VMEM((2 * half * group, vectors_n, width), F32),
         pltpu.VMEM((rows_n * group, vectors_n, width), F32),
     ]
-    kernel = functools.partial(product_kernel, offsets, bool(degree))
+    kernel = functools.partial(product_kernel, runs, order, bool(degree))
     args = [table, tiles, *col_parts, *row_parts, *degree]
     kept, swap, own, *send = call(
         kernel, out_shape, scratch, 32, args, 4 * tiles.size * vectors_n, 1
@@ -214,13 +215,13 @@
     )
 
 
-def form_kernel(offsets, table, tiles_ref, gram_ref, *refs):
-    col_end = len(offsets[0])
+def form_kernel(runs, table, tiles_ref, gram_ref, *refs):
+    col_end = len(runs[0])
     col_parts, row_parts = refs[:col_end], refs[col_end:-5]
     out_ref, col_panel, row_panel, left, right = refs[-5:]
     _, vectors_n, width = col_panel.shape
-    fill(col_panel, col_parts, offsets[0])
-    fill(row_panel, row_parts, offsets[1])
+    fill(col_panel, col_parts, runs[0])
+    fill(row_panel, row_parts, runs[1])
     for t in range(tiles_ref.shape[0]):
         columns = slice(t * width, (t + 1) * width)
         left[:, columns] = row_panel[table[1, t]]
@@ -247,30 +248,19 @@
     row, col = square_index(n)
     table = jnp.concatenate([gram, jnp.where(row == col, 1.0, 0.0)], 1)
     bands = [table[i : i + 8] for i in range(0, n, 8)]
-    line = lax.broadcasted_iota(jnp.int32, (8, 2 * n), 0)
-    for j in range(0, n, 2):
-        at, low = j // 8, j % 8
-        one = bands[at][low : low + 1, :]
-        two = bands[at][low + 1 : low + 2, :]
-        a, b, c = one[:, j : j + 1], one[:, j + 1 : j + 2], two[:, j + 1 : j + 2]
-        scale = 1.0 / (a * c - b * b)
-        to_one = (c * scale) * one - (b * scale) * two
-        to_two = (a * scale) * two - (b * scale) * one
+    below = lax.broadcasted_iota(jnp.int32, (8, 2 * n), 0)
+    for j in range(n):
+        at, line = j // 8, j % 8
+        pivot_row = bands[at][line : line + 1, :]
+        pivot_row = jnp.broadcast_to(pivot_row / pivot_row[:, j : j + 1], (8, 2 * n))
         for i in range(at, n // 8):
-            update = bands[i][:, j : j + 1] * to_one + bands[i][:, j + 1 : j + 2] * to_two
+            update = bands[i][:, j : j + 1] * pivot_row
             if i == at:
-                update = jnp.where(line > low + 1, update, 0.0)
+                update = jnp.where(below > line, update, 0.0)
             bands[i] = bands[i] - update
     table = jnp.concatenate(bands, 0)
-    left, right = table[:, :n], table[:, n:]
-    pivots = jnp.sum(jnp.where(row == col, left, 0.0), 1, keepdims=True)
-    beside = jnp.sum(jnp.where(row + 1 == col, left, 0.0), 1, keepdims=True)
-    odd = row % 2 == 1
-    ratio = beside / pivots
-    above = pltpu.roll(jnp.broadcast_to(ratio, (n, n)), 1, 0)
-    right = jnp.where(odd, right - above * pltpu.roll(right, 1, 0), right)
-    cut = pltpu.roll(jnp.broadcast_to(ratio * beside, (n, n)), 1, 0)
-    return right / jnp.sqrt(jnp.where(odd, pivots - cut, pivots))
+    pivots = jnp.sum(jnp.where(row == col, table[:, :n], 0.0), 1, keepdims=True)
+    return table[:, n:] / jnp.sqrt(pivots)
 
 
 def last_kernel(total_nodes, filtered_ref, *refs):
@@ -322,28 +312,38 @@
     table = jnp.stack([col_apart, row_apart, row_halves]) * group
     table = (table + jnp.stack([tile_cols, tile_rows, tile_rows]) % group).astype(jnp.int32)
 
-    col_offsets, d = [0], rows_n // 2
-    while d:
-        col_offsets += [offset ^ d for offset in col_offsets]
-        d //= 2
-    row_offsets = [2 * d + core for core in range(2) for d in range(chips_n)]
-    offsets = (col_offsets, row_offsets)
-
-    def gather(rounded):
-        held, d = [rounded], rows_n // 2
-        while d:
-            near = trade(rounded, "row", d)
-            if len(held) > 1:
-                near, *rest = lax.optimization_barrier((near, *held[1:]))
-                held = [rounded, *rest]
-            held += [near, *(trade(part, "row", d) for part in held[1:])]
-            d //= 2
+    late = 1
+    levels = [rows_n >> i for i in range(1, rows_n.bit_length())]
+    col_runs = [[(0, group)]]
+    for d in levels:
+        if len(col_runs) == 1:
+            col_runs += [[(d * group, group)]]
+            continue
+        cut = group - late
+        passed = [((p // group ^ d) * group + p % group, n) for run in col_runs[1:] for p, n in run]
+        col_runs += [[(d * group, cut)], [(d * group + cut, late), *passed]]
+    row_runs = [[((2 * d + core) * group, group)] for core in range(2) for d in range(chips_n)]
+    runs = (col_runs, row_runs)
+    order = [*range(rows_n // 2, rows_n), *range(1, rows_n // 2)]
+
+    def gather(rounded, first=()):
+        held = [rounded]
+        for d in levels:
+            if len(held) == 1:
+                held += [trade(rounded, "row", d)]
+                continue
+            near = trade(rounded[: group - late], "row", d)
+            near, *passed = lax.optimization_barrier((near, *held[1:], *first))
+            held[1:] = passed[: len(held) - 1]
+            held += [near, trade(jnp.concatenate([rounded[group - late :], *held[1:]]), "row", d)]
         chips = [rounded, *exchange([rounded] * (chips_n - 1), "col", 2)]
         return held, chips + [trade(chip, "col", 1) for chip in chips]
 
     def apply(rounded, degree=()):
-        kept, swap, col_own, col_send = products(tiles, table, *gather(rounded), offsets, degree)
-        col_got = exchange(col_send, "row")
+        kept, swap, col_own, col_send = products(
+            tiles, table, *gather(rounded, degree), runs, order, degree
+        )
+        col_got = [trade(part, "row", d) for d, part in zip(order, col_send)]
         row_own, *row_send = merge(kept, trade(swap, "col", 1), degree)
         if degree:
             own_degree, *row_send = row_send
@@ -377,7 +377,7 @@
     )
     col_parts, row_parts = gather(rounded)
     sums = call(
-        functools.partial(form_kernel, offsets),
+        functools.partial(form_kernel, runs),
         jax.ShapeDtypeStruct((vectors_n // 2 + 8, 2 * vectors_n), F32),
         [
             pltpu.VMEM((rows_n * group, vectors_n, width), BF16),

time: 116 us -> 113 us (0.974)
  starting transfers between devices: 55.8 us -> 53.2 us
  Pallas kernels: 17.5 us -> 15.7 us
    ppermute x51, starting transfers between devices: 55.8 us -> 53.2 us  [trade(): return lax.ppermute(part, axis, [(i, i ^ d) for i in range(n)])]
    pallas_call x10, Pallas kernels: 17.5 us -> 15.7 us  [call(): pl.pallas_call(kernel, out_shape=out_shape, in_specs=[SMEM] * smem + [VME...]
  transfers between devices with their start and end apart: 51 -> 51, of which waited for: 27 -> 26; matrix products, arithmetic and copies ran while one was open for 0% -> 0% of each run, Pallas kernels for 2% -> 2%
where the time goes in v8:
time: 113 us
  starting transfers between devices  53.2 us (47%)
  waiting for transfers between devices  39.7 us (35%)
  Pallas kernels  15.7 us (14%)
  local copies, waits for them, and re-layouts  3.5 us (3%)
    ppermute x51, starting transfers between devices, trade(): return lax.ppermute(part, axis, [(i, i ^ d) for i in range(n)])  53.2 us
    ppermute x51, waiting for transfers between devices, trade(): return lax.ppermute(part, axis, [(i, i ^ d) for i in range(n)])  39.7 us
    pallas_call x10, Pallas kernels, call(): pl.pallas_call(kernel, out_shape=out_shape, in_specs=[SMEM] * smem + [VME...  15.7 us
    unnamed x12, local copies, waits for them, and re-layouts  3.46 us
  transfers between devices with their start and end apart: 51, of which 26 were waited for; matrix products, arithmetic and copies ran while one was open for 0% of the time, Pallas kernels for 2%

profile of v8, /device:TPU:0, one launch (start us, length us, event | category | flops | bytes accessed | tf_op | source)
XLA Modules:
  0.0 113.0 jit_solution(12947104721177966690)
XLA Ops:
  0.6 0.9 copy-done.2
  1.6 4.0 %collective-permute-start.5 = (bf16[8,64,128]{2,1,0:T(8,128)(2,1)S(1)}, bf16[8,64,128]{2,1,0:T(8,128)(2,1)S(1)}, u32[]{:S(2)}, u32[]{:S(2)}) collective-permute-start(bf16[8,64,128]{2,1,0:T(8,128)(2,1)S(1)} %shard_map.59.refs_0_.refs_4_), channel_id=1, source_target_pairs={{0,6},{1,7},{2,4},{3,5},{4,2},{5,3},{6,0},{7,1},{8,14},{9,15},{10,... | collective-permute-start | bytes 393224 | tf_op jit(solution)/shard_map/ppermute | solution.py:37
  6.2 3.0 %collective-permute-start.1 = (bf16[8,64,128]{2,1,0:T(8,128)(2,1)S(1)}, bf16[8,64,128]{2,1,0:T(8,128)(2,1)S(1)}, u32[]{:S(2)}, u32[]{:S(2)}) collective-permute-start(bf16[8,64,128]{2,1,0:T(8,128)(2,1)S(1)} %shard_map.59.refs_0_.refs_4_), channel_id=1, source_target_pairs={{0,16},{8,24},{16,0},{24,8},{1,17},{9,25},{17,1},{25,9},{2,18},{10... | collective-permute-start | bytes 393224 | tf_op jit(solution)/shard_map/ppermute | solution.py:37
  9.2 1.6 %collective-permute-start = (bf16[7,64,128]{2,1,0:T(8,128)(2,1)S(1)}, bf16[7,64,128]{2,1,0:T(8,128)(2,1)S(1)}, u32[]{:S(2)}, u32[]{:S(2)}) collective-permute-start(bf16[7,64,128]{2,1,0:T(8,128)(2,1)S(1)} %slice.24), channel_id=1, source_target_pairs={{0,8},{8,0},{16,24},{24,16},{1,9},{9,1},{17,25},{25,17},{2,10},{10... | collective-permute-start | bytes 344072 | tf_op jit(solution)/shard_map/ppermute | solution.py:37
  12.2 1.2 %copy-done = bf16[1,1,32,128,128]{4,3,2,1,0:T(8,128)(2,1)S(1)} copy-done((bf16[1,1,32,128,128]{4,3,2,1,0:T(8,128)(2,1)S(1)}, bf16[1,1,32,128,128]{4,3,2,1,0:T(8,128)(2,1)}, u32[]{:S(2)}) %copy-start) | copy-done | bytes 1048600
  13.4 1.5 %shard_map.60 = (f32[64,128]{1,0:T(8,128)S(1)}, f32[32,128]{1,0:T(8,128)S(1)}) custom-call(s32[3,32]{1,0:T(4,128)S(1)} %fusion.1.table, bf16[32,128,128]{2,1,0:T(8,128)(2,1)S(1)} %bitcast.6), custom_call_target="tpu_custom_call" | custom-call | flops 33554432 | bytes 1048960 | tf_op jit(solution)/shard_map/pallas_call | solution.py:24
  15.0 1.1 collective-permute-start.2
  18.2 2.0 %collective-permute-done.2.refs_3_ = bf16[9,64,128]{2,1,0:T(8,128)(2,1)S(1)} collective-permute-done((bf16[9,64,128]{2,1,0:T(8,128)(2,1)S(1)}, bf16[9,64,128]{2,1,0:T(8,128)(2,1)S(1)}, u32[]{:S(2)}, u32[]{:S(2)}) %collective-permute-start.2) | collective-permute-done | bytes 147488 | tf_op jit(solution)/shard_map/ppermute | solution.py:37
  20.2 1.9 %shard_map.61 = (f32[4,8,64,128]{3,2,1,0:T(8,128)S(1)}, bf16[4,528,128]{2,1,0:T(8,128)(2,1)S(1)}, f32[8,64,128]{2,1,0:T(8,128)S(1)}, bf16[528,128]{1,0:T(8,128)(...) custom-call(s32[3,32]{1,0:T(4,128)S(1)} %fusion.1.table, bf16[32,128,128]{2,1,0:T(8,128)(2,1)S(1)} %bitcast.7, ...), custom_call_target="tpu_custom_call" | custom-call | flops 134217728 | bytes 2670976 | tf_op jit(solution)/shard_map/pallas_call | solution.py:24
  22.2 2.1 %collective-permute-start.14 = (bf16[528,128]{1,0:T(8,128)(2,1)S(1)}, bf16[528,128]{1,0:T(8,128)(2,1)S(1)}, u32[]{:S(2)}, u32[]{:S(2)}) collective-permute-start(bf16[528,128]{1,0:T(8,128)(2,1)S(1)} %get-tuple-element.49), channel_id=1, source_target_pairs={{0,16},{8,24},{16,0},{24,8},{1,17},{9,25},{17,1},{25,9},{2,18},{10... | collective-permute-start | bytes 405512 | tf_op jit(solution)/shard_map/ppermute | solution.py:37
  24.3 1.4 %collective-permute-start.15 = (bf16[528,128]{1,0:T(8,128)(2,1)S(1)}, bf16[528,128]{1,0:T(8,128)(2,1)S(1)}, u32[]{:S(2)}, u32[]{:S(2)}) collective-permute-start(bf16[528,128]{1,0:T(8,128)(2,1)S(1)} %get-tuple-element.50), channel_id=1, source_target_pairs={{0,24},{8,16},{16,8},{24,0},{1,25},{9,17},{17,9},{25,1},{2,26},{10... | collective-permute-start | bytes 405512 | tf_op jit(solution)/shard_map/ppermute | solution.py:37
  26.2 1.6 %collective-permute-start.11 = (bf16[528,128]{1,0:T(8,128)(2,1)S(1)}, bf16[528,128]{1,0:T(8,128)(2,1)S(1)}, u32[]{:S(2)}, u32[]{:S(2)}) collective-permute-start(bf16[528,128]{1,0:T(8,128)(2,1)S(1)} %get-tuple-element.46), channel_id=1, source_target_pairs={{0,2},{1,3},{2,0},{3,1},{4,6},{5,7},{6,4},{7,5},{8,10},{9,11},{10,... | collective-permute-start | bytes 405512 | tf_op jit(solution)/shard_map/ppermute | solution.py:37
  27.7 1.5 %collective-permute-start.12 = (bf16[528,128]{1,0:T(8,128)(2,1)S(1)}, bf16[528,128]{1,0:T(8,128)(2,1)S(1)}, u32[]{:S(2)}, u32[]{:S(2)}) collective-permute-start(bf16[528,128]{1,0:T(8,128)(2,1)S(1)} %get-tuple-element.47), channel_id=1, source_target_pairs={{0,4},{1,5},{2,6},{3,7},{4,0},{5,1},{6,2},{7,3},{8,12},{9,13},{10,... | collective-permute-start | bytes 405512 | tf_op jit(solution)/shard_map/ppermute | solution.py:37
  29.2 6.1 %collective-permute-done.14.refs_3_ = bf16[528,128]{1,0:T(8,128)(2,1)S(1)} collective-permute-done((bf16[528,128]{1,0:T(8,128)(2,1)S(1)}, bf16[528,128]{1,0:T(8,128)(2,1)S(1)}, u32[]{:S(2)}, u32[]{:S(2)}) %collective-permute-start.14) | collective-permute-done | bytes 135200 | tf_op jit(solution)/shard_map/ppermute | solution.py:37
  35.4 2.4 %collective-permute-start.13 = (bf16[528,128]{1,0:T(8,128)(2,1)S(1)}, bf16[528,128]{1,0:T(8,128)(2,1)S(1)}, u32[]{:S(2)}, u32[]{:S(2)}) collective-permute-start(bf16[528,128]{1,0:T(8,128)(2,1)S(1)} %get-tuple-element.48), channel_id=1, source_target_pairs={{0,6},{1,7},{2,4},{3,5},{4,2},{5,3},{6,0},{7,1},{8,14},{9,15},{10,... | collective-permute-start | bytes 405512 | tf_op jit(solution)/shard_map/ppermute | solution.py:37
  37.9 3.4 %collective-permute-done.13.refs_2_ = bf16[528,128]{1,0:T(8,128)(2,1)S(1)} collective-permute-done((bf16[528,128]{1,0:T(8,128)(2,1)S(1)}, bf16[528,128]{1,0:T(8,128)(2,1)S(1)}, u32[]{:S(2)}, u32[]{:S(2)}) %collective-permute-start.13) | collective-permute-done | bytes 135200 | tf_op jit(solution)/shard_map/ppermute | solution.py:37
  41.6 3.6 %collective-permute-start.17 = (bf16[7,64,128]{2,1,0:T(8,128)(2,1)S(1)}, bf16[7,64,128]{2,1,0:T(8,128)(2,1)S(1)}, u32[]{:S(2)}, u32[]{:S(2)}) collective-permute-start(bf16[7,64,128]{2,1,0:T(8,128)(2,1)S(1)} %slice.20), channel_id=1, source_target_pairs={{0,8},{8,0},{16,24},{24,16},{1,9},{9,1},{17,25},{25,17},{2,10},{10... | collective-permute-start | bytes 344072 | tf_op jit(solution)/shard_map/ppermute | solution.py:37
  45.2 2.4 %collective-permute-start.22 = (bf16[8,64,128]{2,1,0:T(8,128)(2,1)S(1)}, bf16[8,64,128]{2,1,0:T(8,128)(2,1)S(1)}, u32[]{:S(2)}, u32[]{:S(2)}) collective-permute-start(bf16[8,64,128]{2,1,0:T(8,128)(2,1)S(1)} %get-tuple-element.54.refs_0_.refs_4_), channel_id=1, source_target_pairs={{0,6},{1,7},{2,4},{3,5},{4,2},{5,3},{6,0},{7,1},{8,14},{9,15},{10,... | collective-permute-start | bytes 393224 | tf_op jit(solution)/shard_map/ppermute | solution.py:37
  49.0 1.1 %collective-permute-start.19 = (bf16[9,64,128]{2,1,0:T(8,128)(2,1)S(1)}, bf16[9,64,128]{2,1,0:T(8,128)(2,1)S(1)}, u32[]{:S(2)}, u32[]{:S(2)}) collective-permute-start(bf16[9,64,128]{2,1,0:T(8,128)(2,1)S(1)} %pad_maximum_fusion.1), channel_id=1, source_target_pairs={{0,8},{8,0},{16,24},{24,16},{1,9},{9,1},{17,25},{25,17},{2,10},{10... | collective-permute-start | bytes 442376 | tf_op jit(solution)/shard_map/ppermute | solution.py:37
  50.1 2.3 %collective-permute-done.22.refs_7_ = bf16[8,64,128]{2,1,0:T(8,128)(2,1)S(1)} collective-permute-done((bf16[8,64,128]{2,1,0:T(8,128)(2,1)S(1)}, bf16[8,64,128]{2,1,0:T(8,128)(2,1)S(1)}, u32[]{:S(2)}, u32[]{:S(2)}) %collective-permute-start.22) | collective-permute-done | bytes 131104 | tf_op jit(solution)/shard_map/ppermute | solution.py:37
  53.8 0.8 collective-permute-done.25.refs_10_
  54.8 1.9 %shard_map.64 = (f32[4,8,64,128]{3,2,1,0:T(8,128)S(1)}, bf16[4,512,128]{2,1,0:T(8,128)(2,1)S(1)}, f32[8,64,128]{2,1,0:T(8,128)S(1)}, bf16[512,128]{1,0:T(8,128)(...) custom-call(s32[3,32]{1,0:T(4,128)S(1)} %fusion.1.table, bf16[32,128,128]{2,1,0:T(8,128)(2,1)S(1)} %bitcast.8, ...), custom_call_target="tpu_custom_call" | custom-call | flops 134217728 | bytes 2621824 | tf_op jit(solution)/shard_map/pallas_call | solution.py:24
  57.0 0.9 collective-permute-start.31
  58.0 1.7 %collective-permute-start.32 = (bf16[512,128]{1,0:T(8,128)(2,1)S(1)}, bf16[512,128]{1,0:T(8,128)(2,1)S(1)}, u32[]{:S(2)}, u32[]{:S(2)}) collective-permute-start(bf16[512,128]{1,0:T(8,128)(2,1)S(1)} %get-tuple-element.65), channel_id=1, source_target_pairs={{0,24},{8,16},{16,8},{24,0},{1,25},{9,17},{17,9},{25,1},{2,26},{10... | collective-permute-start | bytes 393224 | tf_op jit(solution)/shard_map/ppermute | solution.py:37
  59.6 0.9 collective-permute-start.33
  60.7 1.3 %collective-permute-start.28 = (bf16[512,128]{1,0:T(8,128)(2,1)S(1)}, bf16[512,128]{1,0:T(8,128)(2,1)S(1)}, u32[]{:S(2)}, u32[]{:S(2)}) collective-permute-start(bf16[512,128]{1,0:T(8,128)(2,1)S(1)} %get-tuple-element.61), channel_id=1, source_target_pairs={{0,2},{1,3},{2,0},{3,1},{4,6},{5,7},{6,4},{7,5},{8,10},{9,11},{10,... | collective-permute-start | bytes 393224 | tf_op jit(solution)/shard_map/ppermute | solution.py:37
  61.9 1.3 %collective-permute-start.29 = (bf16[512,128]{1,0:T(8,128)(2,1)S(1)}, bf16[512,128]{1,0:T(8,128)(2,1)S(1)}, u32[]{:S(2)}, u32[]{:S(2)}) collective-permute-start(bf16[512,128]{1,0:T(8,128)(2,1)S(1)} %get-tuple-element.62), channel_id=1, source_target_pairs={{0,4},{1,5},{2,6},{3,7},{4,0},{5,1},{6,2},{7,3},{8,12},{9,13},{10,... | collective-permute-start | bytes 393224 | tf_op jit(solution)/shard_map/ppermute | solution.py:37
  63.2 6.1 %collective-permute-done.31.refs_3_ = bf16[512,128]{1,0:T(8,128)(2,1)S(1)} collective-permute-done((bf16[512,128]{1,0:T(8,128)(2,1)S(1)}, bf16[512,128]{1,0:T(8,128)(2,1)S(1)}, u32[]{:S(2)}, u32[]{:S(2)}) %collective-permute-start.31) | collective-permute-done | bytes 131104 | tf_op jit(solution)/shard_map/ppermute | solution.py:37
  69.3 2.2 %collective-permute-start.30 = (bf16[512,128]{1,0:T(8,128)(2,1)S(1)}, bf16[512,128]{1,0:T(8,128)(2,1)S(1)}, u32[]{:S(2)}, u32[]{:S(2)}) collective-permute-start(bf16[512,128]{1,0:T(8,128)(2,1)S(1)} %get-tuple-element.63), channel_id=1, source_target_pairs={{0,6},{1,7},{2,4},{3,5},{4,2},{5,3},{6,0},{7,1},{8,14},{9,15},{10,... | collective-permute-start | bytes 393224 | tf_op jit(solution)/shard_map/ppermute | solution.py:37
  71.5 4.0 %collective-permute-done.30.refs_2_ = bf16[512,128]{1,0:T(8,128)(2,1)S(1)} collective-permute-done((bf16[512,128]{1,0:T(8,128)(2,1)S(1)}, bf16[512,128]{1,0:T(8,128)(2,1)S(1)}, u32[]{:S(2)}, u32[]{:S(2)}) %collective-permute-start.30) | collective-permute-done | bytes 131104 | tf_op jit(solution)/shard_map/ppermute | solution.py:37
  76.4 2.7 %collective-permute-start.34 = (bf16[7,64,128]{2,1,0:T(8,128)(2,1)S(1)}, bf16[7,64,128]{2,1,0:T(8,128)(2,1)S(1)}, u32[]{:S(2)}, u32[]{:S(2)}) collective-permute-start(bf16[7,64,128]{2,1,0:T(8,128)(2,1)S(1)} %slice.22), channel_id=1, source_target_pairs={{0,8},{8,0},{16,24},{24,16},{1,9},{9,1},{17,25},{25,17},{2,10},{10... | collective-permute-start | bytes 344072 | tf_op jit(solution)/shard_map/ppermute | solution.py:37
  79.1 2.4 %collective-permute-start.39 = (bf16[8,64,128]{2,1,0:T(8,128)(2,1)S(1)}, bf16[8,64,128]{2,1,0:T(8,128)(2,1)S(1)}, u32[]{:S(2)}, u32[]{:S(2)}) collective-permute-start(bf16[8,64,128]{2,1,0:T(8,128)(2,1)S(1)} %get-tuple-element.69.refs_0_.refs_4_), channel_id=1, source_target_pairs={{0,6},{1,7},{2,4},{3,5},{4,2},{5,3},{6,0},{7,1},{8,14},{9,15},{10,... | collective-permute-start | bytes 393224 | tf_op jit(solution)/shard_map/ppermute | solution.py:37
  82.6 1.7 %collective-permute-done.34.refs_2_ = bf16[7,64,128]{2,1,0:T(8,128)(2,1)S(1)} collective-permute-done((bf16[7,64,128]{2,1,0:T(8,128)(2,1)S(1)}, bf16[7,64,128]{2,1,0:T(8,128)(2,1)S(1)}, u32[]{:S(2)}, u32[]{:S(2)}) %collective-permute-start.34) | collective-permute-done | bytes 114720 | tf_op jit(solution)/shard_map/ppermute | solution.py:37
  84.5 1.8 %collective-permute-done.39.refs_7_ = bf16[8,64,128]{2,1,0:T(8,128)(2,1)S(1)} collective-permute-done((bf16[8,64,128]{2,1,0:T(8,128)(2,1)S(1)}, bf16[8,64,128]{2,1,0:T(8,128)(2,1)S(1)}, u32[]{:S(2)}, u32[]{:S(2)}) %collective-permute-start.39) | collective-permute-done | bytes 131104 | tf_op jit(solution)/shard_map/ppermute | solution.py:37
  87.7 0.8 collective-permute-done.42.refs_10_
  88.7 0.9 collective-permute-done.36.refs_3_
  89.6 2.0 %shard_map.67 = f32[40,128]{1,0:T(8,128)S(1)} custom-call(s32[3,32]{1,0:T(4,128)S(1)} %fusion.1.table, bf16[32,128,128]{2,1,0:T(8,128)(2,1)S(1)} %bitcast.9, f32[64,128]{1,0:T(8,128)S(1)} %get-tuple-element.68.gram_ref, bf16[8,64,128]{2,1,0:T(8,128)(2,1)S(1)} %get-tuple-element.69.refs_0_.refs_4_, bf16[8,64,128]{2,1,0:T(8,128)(2,1)S(1)} %collective-permute-done.35.refs_1_, ...), custom_call_target="tpu_custom_call" | custom-call | flops 134217728 | bytes 2654592 | tf_op jit(solution)/shard_map/pallas_call | solution.py:24
  91.6 1.2 %collective-permute-done.44 = f32[40,128]{1,0:T(8,128)S(1)} collective-permute-done((f32[40,128]{1,0:T(8,128)S(1)}, f32[40,128]{1,0:T(8,128)S(1)}, u32[]{:S(2)}, u32[]{:S(2)}) %collective-permute-start.44) | collective-permute-done | bytes 20512 | tf_op jit(solution)/shard_map/ppermute | solution.py:37
  92.8 1.2 %collective-permute-start.47 = (f32[40,128]{1,0:T(8,128)S(1)}, f32[40,128]{1,0:T(8,128)S(1)}, u32[]{:S(2)}, u32[]{:S(2)}) collective-permute-start(f32[40,128]{1,0:T(8,128)S(1)} %add.76), channel_id=1, source_target_pairs={{0,6},{1,7},{2,4},{3,5},{4,2},{5,3},{6,0},{7,1},{8,14},{9,15},{10,... | collective-permute-start | bytes 61448 | tf_op jit(solution)/shard_map/ppermute | solution.py:37
  94.0 0.8 collective-permute-start.46
  94.8 1.5 %collective-permute-start.45 = (f32[40,128]{1,0:T(8,128)S(1)}, f32[40,128]{1,0:T(8,128)S(1)}, u32[]{:S(2)}, u32[]{:S(2)}) collective-permute-start(f32[40,128]{1,0:T(8,128)S(1)} %add.76), channel_id=1, source_target_pairs={{0,2},{1,3},{2,0},{3,1},{4,6},{5,7},{6,4},{7,5},{8,10},{9,11},{10,... | collective-permute-start | bytes 61448 | tf_op jit(solution)/shard_map/ppermute | solution.py:37
  96.3 1.2 %collective-permute-done.47 = f32[40,128]{1,0:T(8,128)S(1)} collective-permute-done((f32[40,128]{1,0:T(8,128)S(1)}, f32[40,128]{1,0:T(8,128)S(1)}, u32[]{:S(2)}, u32[]{:S(2)}) %collective-permute-start.47) | collective-permute-done | bytes 20512 | tf_op jit(solution)/shard_map/ppermute | solution.py:37
  97.8 0.8 collective-permute-done.45
  98.6 2.5 %collective-permute-start.50 = (f32[40,128]{1,0:T(8,128)S(1)}, f32[40,128]{1,0:T(8,128)S(1)}, u32[]{:S(2)}, u32[]{:S(2)}) collective-permute-start(f32[40,128]{1,0:T(8,128)S(1)} %add_add_fusion.refs_0_), channel_id=1, source_target_pairs={{0,24},{8,16},{16,8},{24,0},{1,25},{9,17},{17,9},{25,1},{2,26},{10... | collective-permute-start | bytes 61448 | tf_op jit(solution)/shard_map/ppermute | solution.py:37
  101.2 1.9 %collective-permute-start.48 = (f32[40,128]{1,0:T(8,128)S(1)}, f32[40,128]{1,0:T(8,128)S(1)}, u32[]{:S(2)}, u32[]{:S(2)}) collective-permute-start(f32[40,128]{1,0:T(8,128)S(1)} %add_add_fusion.refs_0_), channel_id=1, source_target_pairs={{0,8},{8,0},{16,24},{24,16},{1,9},{9,1},{17,25},{25,17},{2,10},{10... | collective-permute-start | bytes 61448 | tf_op jit(solution)/shard_map/ppermute | solution.py:37
  103.1 1.4 %collective-permute-done.50.refs_3_ = f32[40,128]{1,0:T(8,128)S(1)} collective-permute-done((f32[40,128]{1,0:T(8,128)S(1)}, f32[40,128]{1,0:T(8,128)S(1)}, u32[]{:S(2)}, u32[]{:S(2)}) %collective-permute-start.50) | collective-permute-done | bytes 20512 | tf_op jit(solution)/shard_map/ppermute | solution.py:37
  104.5 1.4 %collective-permute-done.49.refs_2_ = f32[40,128]{1,0:T(8,128)S(1)} collective-permute-done((f32[40,128]{1,0:T(8,128)S(1)}, f32[40,128]{1,0:T(8,128)S(1)}, u32[]{:S(2)}, u32[]{:S(2)}) %collective-permute-start.49) | collective-permute-done | bytes 20512 | tf_op jit(solution)/shard_map/ppermute | solution.py:37
  105.9 7.2 %shard_map.68 = (f32[64,1024]{1,0:T(8,128)}, f32[64,64]{1,0:T(8,128)}) custom-call(f32[64,1024]{1,0:T(8,128)S(1)} %get-tuple-element.67.filtered_ref, f32[40,128]{1,0:T(8,128)S(1)} %add_add_fusion.refs_0_, f32[40,128]{1,0:T(8,128)S(1)} %collective-permute-done.48.refs_1_, f32[40,128]{1,0:T(8,128)S(1)} %collective-permute-done.49.refs_2_, ...), custom_call_target="tpu_custom_call" | custom-call | bytes 344064 | tf_op jit(solution)/shard_map/pallas_call | solution.py:24
  (90 shorter events, 12.2 us)
Async XLA Ops:
  1.6 14.5 %collective-permute-start.5 = (bf16[8,64,128]{2,1,0:T(8,128)(2,1)S(1)}, bf16[8,64,128]{2,1,0:T(8,128)(2,1)S(1)}, u32[]{:S(2)}, u32[]{:S(2)}) collective-permute-start(bf16[8,64,128]{2,1,0:T(8,128)(2,1)S(1)} %shard_map.59.refs_0_.refs_4_), channel_id=1, source_target_pairs={{0,6},{1,7},{2,4},{3,5},{4,2},{5,3},{6,0},{7,1},{8,14},{9,15},{10,... | collective-permute-start | bytes 393224 | tf_op jit(solution)/shard_map/ppermute | solution.py:37
  5.6 11.1 %collective-permute-start.4 = (bf16[8,64,128]{2,1,0:T(8,128)(2,1)S(1)}, bf16[8,64,128]{2,1,0:T(8,128)(2,1)S(1)}, u32[]{:S(2)}, u32[]{:S(2)}) collective-permute-start(bf16[8,64,128]{2,1,0:T(8,128)(2,1)S(1)} %shard_map.59.refs_0_.refs_4_), channel_id=1, source_target_pairs={{0,4},{1,5},{2,6},{3,7},{4,0},{5,1},{6,2},{7,3},{8,12},{9,13},{10,... | collective-permute-start | bytes 393224 | tf_op jit(solution)/shard_map/ppermute | solution.py:37
  6.1 10.7 %collective-permute-start.3 = (bf16[8,64,128]{2,1,0:T(8,128)(2,1)S(1)}, bf16[8,64,128]{2,1,0:T(8,128)(2,1)S(1)}, u32[]{:S(2)}, u32[]{:S(2)}) collective-permute-start(bf16[8,64,128]{2,1,0:T(8,128)(2,1)S(1)} %shard_map.59.refs_0_.refs_4_), channel_id=1, source_target_pairs={{0,2},{1,3},{2,0},{3,1},{4,6},{5,7},{6,4},{7,5},{8,10},{9,11},{10,... | collective-permute-start | bytes 393224 | tf_op jit(solution)/shard_map/ppermute | solution.py:37
  6.2 8.8 %collective-permute-start.1 = (bf16[8,64,128]{2,1,0:T(8,128)(2,1)S(1)}, bf16[8,64,128]{2,1,0:T(8,128)(2,1)S(1)}, u32[]{:S(2)}, u32[]{:S(2)}) collective-permute-start(bf16[8,64,128]{2,1,0:T(8,128)(2,1)S(1)} %shard_map.59.refs_0_.refs_4_), channel_id=1, source_target_pairs={{0,16},{8,24},{16,0},{24,8},{1,17},{9,25},{17,1},{25,9},{2,18},{10... | collective-permute-start | bytes 393224 | tf_op jit(solution)/shard_map/ppermute | solution.py:37
  9.2 5.8 %collective-permute-start = (bf16[7,64,128]{2,1,0:T(8,128)(2,1)S(1)}, bf16[7,64,128]{2,1,0:T(8,128)(2,1)S(1)}, u32[]{:S(2)}, u32[]{:S(2)}) collective-permute-start(bf16[7,64,128]{2,1,0:T(8,128)(2,1)S(1)} %slice.24), channel_id=1, source_target_pairs={{0,8},{8,0},{16,24},{24,16},{1,9},{9,1},{17,25},{25,17},{2,10},{10... | collective-permute-start | bytes 344072 | tf_op jit(solution)/shard_map/ppermute | solution.py:37
  15.0 5.2 %collective-permute-start.2 = (bf16[9,64,128]{2,1,0:T(8,128)(2,1)S(1)}, bf16[9,64,128]{2,1,0:T(8,128)(2,1)S(1)}, u32[]{:S(2)}, u32[]{:S(2)}) collective-permute-start(bf16[9,64,128]{2,1,0:T(8,128)(2,1)S(1)} %pad_maximum_fusion), channel_id=1, source_target_pairs={{0,8},{8,0},{16,24},{24,16},{1,9},{9,1},{17,25},{25,17},{2,10},{10... | collective-permute-start | bytes 442376 | tf_op jit(solution)/shard_map/ppermute | solution.py:37
  16.1 1.3 %collective-permute-start.6 = (bf16[8,64,128]{2,1,0:T(8,128)(2,1)S(1)}, bf16[8,64,128]{2,1,0:T(8,128)(2,1)S(1)}, u32[]{:S(2)}, u32[]{:S(2)}) collective-permute-start(bf16[8,64,128]{2,1,0:T(8,128)(2,1)S(1)} %shard_map.59.refs_0_.refs_4_), channel_id=1, source_target_pairs={{0,1},{1,0},{2,3},{3,2},{4,5},{5,4},{6,7},{7,6},{8,9},{9,8},{10,11... | collective-permute-start | bytes 393224 | tf_op jit(solution)/shard_map/ppermute | solution.py:37
  16.1 1.5 %collective-permute-start.9 = (bf16[8,64,128]{2,1,0:T(8,128)(2,1)S(1)}, bf16[8,64,128]{2,1,0:T(8,128)(2,1)S(1)}, u32[]{:S(2)}, u32[]{:S(2)}) collective-permute-start(bf16[8,64,128]{2,1,0:T(8,128)(2,1)S(1)} %collective-permute-done.5.refs_7_), channel_id=1, source_target_pairs={{0,1},{1,0},{2,3},{3,2},{4,5},{5,4},{6,7},{7,6},{8,9},{9,8},{10,11... | collective-permute-start | bytes 393224 | tf_op jit(solution)/shard_map/ppermute | solution.py:37
  16.7 1.3 %collective-permute-start.8 = (bf16[8,64,128]{2,1,0:T(8,128)(2,1)S(1)}, bf16[8,64,128]{2,1,0:T(8,128)(2,1)S(1)}, u32[]{:S(2)}, u32[]{:S(2)}) collective-permute-start(bf16[8,64,128]{2,1,0:T(8,128)(2,1)S(1)} %collective-permute-done.4.refs_6_), channel_id=1, source_target_pairs={{0,1},{1,0},{2,3},{3,2},{4,5},{5,4},{6,7},{7,6},{8,9},{9,8},{10,11... | collective-permute-start | bytes 393224 | tf_op jit(solution)/shard_map/ppermute | solution.py:37
  16.7 1.5 %collective-permute-start.7 = (bf16[8,64,128]{2,1,0:T(8,128)(2,1)S(1)}, bf16[8,64,128]{2,1,0:T(8,128)(2,1)S(1)}, u32[]{:S(2)}, u32[]{:S(2)}) collective-permute-start(bf16[8,64,128]{2,1,0:T(8,128)(2,1)S(1)} %collective-permute-done.3.refs_5_), channel_id=1, source_target_pairs={{0,1},{1,0},{2,3},{3,2},{4,5},{5,4},{6,7},{7,6},{8,9},{9,8},{10,11... | collective-permute-start | bytes 393224 | tf_op jit(solution)/shard_map/ppermute | solution.py:37
  22.1 3.9 %collective-permute-start.10 = (bf16[4,528,128]{2,1,0:T(8,128)(2,1)S(1)}, bf16[4,528,128]{2,1,0:T(8,128)(2,1)S(1)}, u32[]{:S(2)}, u32[]{:S(2)}) collective-permute-start(bf16[4,528,128]{2,1,0:T(8,128)(2,1)S(1)} %get-tuple-element.42), channel_id=1, source_target_pairs={{0,1},{1,0},{2,3},{3,2},{4,5},{5,4},{6,7},{7,6},{8,9},{9,8},{10,11... | collective-permute-start | bytes 1622024 | tf_op jit(solution)/shard_map/ppermute | solution.py:37
  22.2 13.2 %collective-permute-start.14 = (bf16[528,128]{1,0:T(8,128)(2,1)S(1)}, bf16[528,128]{1,0:T(8,128)(2,1)S(1)}, u32[]{:S(2)}, u32[]{:S(2)}) collective-permute-start(bf16[528,128]{1,0:T(8,128)(2,1)S(1)} %get-tuple-element.49), channel_id=1, source_target_pairs={{0,16},{8,24},{16,0},{24,8},{1,17},{9,25},{17,1},{25,9},{2,18},{10... | collective-permute-start | bytes 405512 | tf_op jit(solution)/shard_map/ppermute | solution.py:37
  24.3 13.5 %collective-permute-start.15 = (bf16[528,128]{1,0:T(8,128)(2,1)S(1)}, bf16[528,128]{1,0:T(8,128)(2,1)S(1)}, u32[]{:S(2)}, u32[]{:S(2)}) collective-permute-start(bf16[528,128]{1,0:T(8,128)(2,1)S(1)} %get-tuple-element.50), channel_id=1, source_target_pairs={{0,24},{8,16},{16,8},{24,0},{1,25},{9,17},{17,9},{25,1},{2,26},{10... | collective-permute-start | bytes 405512 | tf_op jit(solution)/shard_map/ppermute | solution.py:37
  25.7 12.2 %collective-permute-start.16 = (bf16[528,128]{1,0:T(8,128)(2,1)S(1)}, bf16[528,128]{1,0:T(8,128)(2,1)S(1)}, u32[]{:S(2)}, u32[]{:S(2)}) collective-permute-start(bf16[528,128]{1,0:T(8,128)(2,1)S(1)} %get-tuple-element.51), channel_id=1, source_target_pairs={{0,8},{8,0},{16,24},{24,16},{1,9},{9,1},{17,25},{25,17},{2,10},{10... | collective-permute-start | bytes 405512 | tf_op jit(solution)/shard_map/ppermute | solution.py:37
  26.2 11.7 %collective-permute-start.11 = (bf16[528,128]{1,0:T(8,128)(2,1)S(1)}, bf16[528,128]{1,0:T(8,128)(2,1)S(1)}, u32[]{:S(2)}, u32[]{:S(2)}) collective-permute-start(bf16[528,128]{1,0:T(8,128)(2,1)S(1)} %get-tuple-element.46), channel_id=1, source_target_pairs={{0,2},{1,3},{2,0},{3,1},{4,6},{5,7},{6,4},{7,5},{8,10},{9,11},{10,... | collective-permute-start | bytes 405512 | tf_op jit(solution)/shard_map/ppermute | solution.py:37
  27.7 10.1 %collective-permute-start.12 = (bf16[528,128]{1,0:T(8,128)(2,1)S(1)}, bf16[528,128]{1,0:T(8,128)(2,1)S(1)}, u32[]{:S(2)}, u32[]{:S(2)}) collective-permute-start(bf16[528,128]{1,0:T(8,128)(2,1)S(1)} %get-tuple-element.47), channel_id=1, source_target_pairs={{0,4},{1,5},{2,6},{3,7},{4,0},{5,1},{6,2},{7,3},{8,12},{9,13},{10,... | collective-permute-start | bytes 405512 | tf_op jit(solution)/shard_map/ppermute | solution.py:37
  35.4 5.9 %collective-permute-start.13 = (bf16[528,128]{1,0:T(8,128)(2,1)S(1)}, bf16[528,128]{1,0:T(8,128)(2,1)S(1)}, u32[]{:S(2)}, u32[]{:S(2)}) collective-permute-start(bf16[528,128]{1,0:T(8,128)(2,1)S(1)} %get-tuple-element.48), channel_id=1, source_target_pairs={{0,6},{1,7},{2,4},{3,5},{4,2},{5,3},{6,0},{7,1},{8,14},{9,15},{10,... | collective-permute-start | bytes 405512 | tf_op jit(solution)/shard_map/ppermute | solution.py:37
  41.5 7.5 %collective-permute-start.18 = (bf16[8,64,128]{2,1,0:T(8,128)(2,1)S(1)}, bf16[8,64,128]{2,1,0:T(8,128)(2,1)S(1)}, u32[]{:S(2)}, u32[]{:S(2)}) collective-permute-start(bf16[8,64,128]{2,1,0:T(8,128)(2,1)S(1)} %get-tuple-element.54.refs_0_.refs_4_), channel_id=1, source_target_pairs={{0,16},{8,24},{16,0},{24,8},{1,17},{9,25},{17,1},{25,9},{2,18},{10... | collective-permute-start | bytes 393224 | tf_op jit(solution)/shard_map/ppermute | solution.py:37
  41.6 7.4 %collective-permute-start.17 = (bf16[7,64,128]{2,1,0:T(8,128)(2,1)S(1)}, bf16[7,64,128]{2,1,0:T(8,128)(2,1)S(1)}, u32[]{:S(2)}, u32[]{:S(2)}) collective-permute-start(bf16[7,64,128]{2,1,0:T(8,128)(2,1)S(1)} %slice.20), channel_id=1, source_target_pairs={{0,8},{8,0},{16,24},{24,16},{1,9},{9,1},{17,25},{25,17},{2,10},{10... | collective-permute-start | bytes 344072 | tf_op jit(solution)/shard_map/ppermute | solution.py:37
  45.2 7.2 %collective-permute-start.22 = (bf16[8,64,128]{2,1,0:T(8,128)(2,1)S(1)}, bf16[8,64,128]{2,1,0:T(8,128)(2,1)S(1)}, u32[]{:S(2)}, u32[]{:S(2)}) collective-permute-start(bf16[8,64,128]{2,1,0:T(8,128)(2,1)S(1)} %get-tuple-element.54.refs_0_.refs_4_), channel_id=1, source_target_pairs={{0,6},{1,7},{2,4},{3,5},{4,2},{5,3},{6,0},{7,1},{8,14},{9,15},{10,... | collective-permute-start | bytes 393224 | tf_op jit(solution)/shard_map/ppermute | solution.py:37
  47.7 5.6 %collective-permute-start.21 = (bf16[8,64,128]{2,1,0:T(8,128)(2,1)S(1)}, bf16[8,64,128]{2,1,0:T(8,128)(2,1)S(1)}, u32[]{:S(2)}, u32[]{:S(2)}) collective-permute-start(bf16[8,64,128]{2,1,0:T(8,128)(2,1)S(1)} %get-tuple-element.54.refs_0_.refs_4_), channel_id=1, source_target_pairs={{0,4},{1,5},{2,6},{3,7},{4,0},{5,1},{6,2},{7,3},{8,12},{9,13},{10,... | collective-permute-start | bytes 393224 | tf_op jit(solution)/shard_map/ppermute | solution.py:37
  48.2 5.1 %collective-permute-start.20 = (bf16[8,64,128]{2,1,0:T(8,128)(2,1)S(1)}, bf16[8,64,128]{2,1,0:T(8,128)(2,1)S(1)}, u32[]{:S(2)}, u32[]{:S(2)}) collective-permute-start(bf16[8,64,128]{2,1,0:T(8,128)(2,1)S(1)} %get-tuple-element.54.refs_0_.refs_4_), channel_id=1, source_target_pairs={{0,2},{1,3},{2,0},{3,1},{4,6},{5,7},{6,4},{7,5},{8,10},{9,11},{10,... | collective-permute-start | bytes 393224 | tf_op jit(solution)/shard_map/ppermute | solution.py:37
  49.0 5.8 %collective-permute-start.19 = (bf16[9,64,128]{2,1,0:T(8,128)(2,1)S(1)}, bf16[9,64,128]{2,1,0:T(8,128)(2,1)S(1)}, u32[]{:S(2)}, u32[]{:S(2)}) collective-permute-start(bf16[9,64,128]{2,1,0:T(8,128)(2,1)S(1)} %pad_maximum_fusion.1), channel_id=1, source_target_pairs={{0,8},{8,0},{16,24},{24,16},{1,9},{9,1},{17,25},{25,17},{2,10},{10... | collective-permute-start | bytes 442376 | tf_op jit(solution)/shard_map/ppermute | solution.py:37
  50.1 3.6 %collective-permute-start.23 = (bf16[8,64,128]{2,1,0:T(8,128)(2,1)S(1)}, bf16[8,64,128]{2,1,0:T(8,128)(2,1)S(1)}, u32[]{:S(2)}, u32[]{:S(2)}) collective-permute-start(bf16[8,64,128]{2,1,0:T(8,128)(2,1)S(1)} %get-tuple-element.54.refs_0_.refs_4_), channel_id=1, source_target_pairs={{0,1},{1,0},{2,3},{3,2},{4,5},{5,4},{6,7},{7,6},{8,9},{9,8},{10,11... | collective-permute-start | bytes 393224 | tf_op jit(solution)/shard_map/ppermute | solution.py:37
  52.4 1.3 %collective-permute-start.26 = (bf16[8,64,128]{2,1,0:T(8,128)(2,1)S(1)}, bf16[8,64,128]{2,1,0:T(8,128)(2,1)S(1)}, u32[]{:S(2)}, u32[]{:S(2)}) collective-permute-start(bf16[8,64,128]{2,1,0:T(8,128)(2,1)S(1)} %collective-permute-done.22.refs_7_), channel_id=1, source_target_pairs={{0,1},{1,0},{2,3},{3,2},{4,5},{5,4},{6,7},{7,6},{8,9},{9,8},{10,11... | collective-permute-start | bytes 393224 | tf_op jit(solution)/shard_map/ppermute | solution.py:37
  53.2 1.3 %collective-permute-start.25 = (bf16[8,64,128]{2,1,0:T(8,128)(2,1)S(1)}, bf16[8,64,128]{2,1,0:T(8,128)(2,1)S(1)}, u32[]{:S(2)}, u32[]{:S(2)}) collective-permute-start(bf16[8,64,128]{2,1,0:T(8,128)(2,1)S(1)} %collective-permute-done.21.refs_6_), channel_id=1, source_target_pairs={{0,1},{1,0},{2,3},{3,2},{4,5},{5,4},{6,7},{7,6},{8,9},{9,8},{10,11... | collective-permute-start | bytes 393224 | tf_op jit(solution)/shard_map/ppermute | solution.py:37
  53.2 1.5 %collective-permute-start.24 = (bf16[8,64,128]{2,1,0:T(8,128)(2,1)S(1)}, bf16[8,64,128]{2,1,0:T(8,128)(2,1)S(1)}, u32[]{:S(2)}, u32[]{:S(2)}) collective-permute-start(bf16[8,64,128]{2,1,0:T(8,128)(2,1)S(1)} %collective-permute-done.20.refs_5_), channel_id=1, source_target_pairs={{0,1},{1,0},{2,3},{3,2},{4,5},{5,4},{6,7},{7,6},{8,9},{9,8},{10,11... | collective-permute-start | bytes 393224 | tf_op jit(solution)/shard_map/ppermute | solution.py:37
  56.7 3.9 %collective-permute-start.27 = (bf16[4,512,128]{2,1,0:T(8,128)(2,1)S(1)}, bf16[4,512,128]{2,1,0:T(8,128)(2,1)S(1)}, u32[]{:S(2)}, u32[]{:S(2)}) collective-permute-start(bf16[4,512,128]{2,1,0:T(8,128)(2,1)S(1)} %get-tuple-element.58), channel_id=1, source_target_pairs={{0,1},{1,0},{2,3},{3,2},{4,5},{5,4},{6,7},{7,6},{8,9},{9,8},{10,11... | collective-permute-start | bytes 1572872 | tf_op jit(solution)/shard_map/ppermute | solution.py:37
  57.0 12.2 %collective-permute-start.31 = (bf16[512,128]{1,0:T(8,128)(2,1)S(1)}, bf16[512,128]{1,0:T(8,128)(2,1)S(1)}, u32[]{:S(2)}, u32[]{:S(2)}) collective-permute-start(bf16[512,128]{1,0:T(8,128)(2,1)S(1)} %get-tuple-element.64), channel_id=1, source_target_pairs={{0,16},{8,24},{16,0},{24,8},{1,17},{9,25},{17,1},{25,9},{2,18},{10... | collective-permute-start | bytes 393224 | tf_op jit(solution)/shard_map/ppermute | solution.py:37
  58.0 13.5 %collective-permute-start.32 = (bf16[512,128]{1,0:T(8,128)(2,1)S(1)}, bf16[512,128]{1,0:T(8,128)(2,1)S(1)}, u32[]{:S(2)}, u32[]{:S(2)}) collective-permute-start(bf16[512,128]{1,0:T(8,128)(2,1)S(1)} %get-tuple-element.65), channel_id=1, source_target_pairs={{0,24},{8,16},{16,8},{24,0},{1,25},{9,17},{17,9},{25,1},{2,26},{10... | collective-permute-start | bytes 393224 | tf_op jit(solution)/shard_map/ppermute | solution.py:37
  59.6 11.9 %collective-permute-start.33 = (bf16[512,128]{1,0:T(8,128)(2,1)S(1)}, bf16[512,128]{1,0:T(8,128)(2,1)S(1)}, u32[]{:S(2)}, u32[]{:S(2)}) collective-permute-start(bf16[512,128]{1,0:T(8,128)(2,1)S(1)} %get-tuple-element.66), channel_id=1, source_target_pairs={{0,8},{8,0},{16,24},{24,16},{1,9},{9,1},{17,25},{25,17},{2,10},{10... | collective-permute-start | bytes 393224 | tf_op jit(solution)/shard_map/ppermute | solution.py:37
  60.7 10.9 %collective-permute-start.28 = (bf16[512,128]{1,0:T(8,128)(2,1)S(1)}, bf16[512,128]{1,0:T(8,128)(2,1)S(1)}, u32[]{:S(2)}, u32[]{:S(2)}) collective-permute-start(bf16[512,128]{1,0:T(8,128)(2,1)S(1)} %get-tuple-element.61), channel_id=1, source_target_pairs={{0,2},{1,3},{2,0},{3,1},{4,6},{5,7},{6,4},{7,5},{8,10},{9,11},{10,... | collective-permute-start | bytes 393224 | tf_op jit(solution)/shard_map/ppermute | solution.py:37
  61.9 9.6 %collective-permute-start.29 = (bf16[512,128]{1,0:T(8,128)(2,1)S(1)}, bf16[512,128]{1,0:T(8,128)(2,1)S(1)}, u32[]{:S(2)}, u32[]{:S(2)}) collective-permute-start(bf16[512,128]{1,0:T(8,128)(2,1)S(1)} %get-tuple-element.62), channel_id=1, source_target_pairs={{0,4},{1,5},{2,6},{3,7},{4,0},{5,1},{6,2},{7,3},{8,12},{9,13},{10,... | collective-permute-start | bytes 393224 | tf_op jit(solution)/shard_map/ppermute | solution.py:37
  69.3 6.3 %collective-permute-start.30 = (bf16[512,128]{1,0:T(8,128)(2,1)S(1)}, bf16[512,128]{1,0:T(8,128)(2,1)S(1)}, u32[]{:S(2)}, u32[]{:S(2)}) collective-permute-start(bf16[512,128]{1,0:T(8,128)(2,1)S(1)} %get-tuple-element.63), channel_id=1, source_target_pairs={{0,6},{1,7},{2,4},{3,5},{4,2},{5,3},{6,0},{7,1},{8,14},{9,15},{10,... | collective-permute-start | bytes 393224 | tf_op jit(solution)/shard_map/ppermute | solution.py:37
  76.3 8.1 %collective-permute-start.35 = (bf16[8,64,128]{2,1,0:T(8,128)(2,1)S(1)}, bf16[8,64,128]{2,1,0:T(8,128)(2,1)S(1)}, u32[]{:S(2)}, u32[]{:S(2)}) collective-permute-start(bf16[8,64,128]{2,1,0:T(8,128)(2,1)S(1)} %get-tuple-element.69.refs_0_.refs_4_), channel_id=1, source_target_pairs={{0,16},{8,24},{16,0},{24,8},{1,17},{9,25},{17,1},{25,9},{2,18},{10... | collective-permute-start | bytes 393224 | tf_op jit(solution)/shard_map/ppermute | solution.py:37
  76.4 8.0 %collective-permute-start.34 = (bf16[7,64,128]{2,1,0:T(8,128)(2,1)S(1)}, bf16[7,64,128]{2,1,0:T(8,128)(2,1)S(1)}, u32[]{:S(2)}, u32[]{:S(2)}) collective-permute-start(bf16[7,64,128]{2,1,0:T(8,128)(2,1)S(1)} %slice.22), channel_id=1, source_target_pairs={{0,8},{8,0},{16,24},{24,16},{1,9},{9,1},{17,25},{25,17},{2,10},{10... | collective-permute-start | bytes 344072 | tf_op jit(solution)/shard_map/ppermute | solution.py:37
  79.1 7.2 %collective-permute-start.39 = (bf16[8,64,128]{2,1,0:T(8,128)(2,1)S(1)}, bf16[8,64,128]{2,1,0:T(8,128)(2,1)S(1)}, u32[]{:S(2)}, u32[]{:S(2)}) collective-permute-start(bf16[8,64,128]{2,1,0:T(8,128)(2,1)S(1)} %get-tuple-element.69.refs_0_.refs_4_), channel_id=1, source_target_pairs={{0,6},{1,7},{2,4},{3,5},{4,2},{5,3},{6,0},{7,1},{8,14},{9,15},{10,... | collective-permute-start | bytes 393224 | tf_op jit(solution)/shard_map/ppermute | solution.py:37
  81.6 5.6 %collective-permute-start.38 = (bf16[8,64,128]{2,1,0:T(8,128)(2,1)S(1)}, bf16[8,64,128]{2,1,0:T(8,128)(2,1)S(1)}, u32[]{:S(2)}, u32[]{:S(2)}) collective-permute-start(bf16[8,64,128]{2,1,0:T(8,128)(2,1)S(1)} %get-tuple-element.69.refs_0_.refs_4_), channel_id=1, source_target_pairs={{0,4},{1,5},{2,6},{3,7},{4,0},{5,1},{6,2},{7,3},{8,12},{9,13},{10,... | collective-permute-start | bytes 393224 | tf_op jit(solution)/shard_map/ppermute | solution.py:37
  82.1 5.1 %collective-permute-start.37 = (bf16[8,64,128]{2,1,0:T(8,128)(2,1)S(1)}, bf16[8,64,128]{2,1,0:T(8,128)(2,1)S(1)}, u32[]{:S(2)}, u32[]{:S(2)}) collective-permute-start(bf16[8,64,128]{2,1,0:T(8,128)(2,1)S(1)} %get-tuple-element.69.refs_0_.refs_4_), channel_id=1, source_target_pairs={{0,2},{1,3},{2,0},{3,1},{4,6},{5,7},{6,4},{7,5},{8,10},{9,11},{10,... | collective-permute-start | bytes 393224 | tf_op jit(solution)/shard_map/ppermute | solution.py:37
  84.4 5.2 %collective-permute-start.36 = (bf16[9,64,128]{2,1,0:T(8,128)(2,1)S(1)}, bf16[9,64,128]{2,1,0:T(8,128)(2,1)S(1)}, u32[]{:S(2)}, u32[]{:S(2)}) collective-permute-start(bf16[9,64,128]{2,1,0:T(8,128)(2,1)S(1)} %pad_maximum_fusion.2), channel_id=1, source_target_pairs={{0,8},{8,0},{16,24},{24,16},{1,9},{9,1},{17,25},{25,17},{2,10},{10... | collective-permute-start | bytes 442376 | tf_op jit(solution)/shard_map/ppermute | solution.py:37
  84.5 3.2 %collective-permute-start.40 = (bf16[8,64,128]{2,1,0:T(8,128)(2,1)S(1)}, bf16[8,64,128]{2,1,0:T(8,128)(2,1)S(1)}, u32[]{:S(2)}, u32[]{:S(2)}) collective-permute-start(bf16[8,64,128]{2,1,0:T(8,128)(2,1)S(1)} %get-tuple-element.69.refs_0_.refs_4_), channel_id=1, source_target_pairs={{0,1},{1,0},{2,3},{3,2},{4,5},{5,4},{6,7},{7,6},{8,9},{9,8},{10,11... | collective-permute-start | bytes 393224 | tf_op jit(solution)/shard_map/ppermute | solution.py:37
  87.1 1.5 %collective-permute-start.41 = (bf16[8,64,128]{2,1,0:T(8,128)(2,1)S(1)}, bf16[8,64,128]{2,1,0:T(8,128)(2,1)S(1)}, u32[]{:S(2)}, u32[]{:S(2)}) collective-permute-start(bf16[8,64,128]{2,1,0:T(8,128)(2,1)S(1)} %collective-permute-done.37.refs_5_), channel_id=1, source_target_pairs={{0,1},{1,0},{2,3},{3,2},{4,5},{5,4},{6,7},{7,6},{8,9},{9,8},{10,11... | collective-permute-start | bytes 393224 | tf_op jit(solution)/shard_map/ppermute | solution.py:37
  92.8 4.7 %collective-permute-start.47 = (f32[40,128]{1,0:T(8,128)S(1)}, f32[40,128]{1,0:T(8,128)S(1)}, u32[]{:S(2)}, u32[]{:S(2)}) collective-permute-start(f32[40,128]{1,0:T(8,128)S(1)} %add.76), channel_id=1, source_target_pairs={{0,6},{1,7},{2,4},{3,5},{4,2},{5,3},{6,0},{7,1},{8,14},{9,15},{10,... | collective-permute-start | bytes 61448 | tf_op jit(solution)/shard_map/ppermute | solution.py:37
  94.0 3.8 %collective-permute-start.46 = (f32[40,128]{1,0:T(8,128)S(1)}, f32[40,128]{1,0:T(8,128)S(1)}, u32[]{:S(2)}, u32[]{:S(2)}) collective-permute-start(f32[40,128]{1,0:T(8,128)S(1)} %add.76), channel_id=1, source_target_pairs={{0,4},{1,5},{2,6},{3,7},{4,0},{5,1},{6,2},{7,3},{8,12},{9,13},{10,... | collective-permute-start | bytes 61448 | tf_op jit(solution)/shard_map/ppermute | solution.py:37
  94.8 3.8 %collective-permute-start.45 = (f32[40,128]{1,0:T(8,128)S(1)}, f32[40,128]{1,0:T(8,128)S(1)}, u32[]{:S(2)}, u32[]{:S(2)}) collective-permute-start(f32[40,128]{1,0:T(8,128)S(1)} %add.76), channel_id=1, source_target_pairs={{0,2},{1,3},{2,0},{3,1},{4,6},{5,7},{6,4},{7,5},{8,10},{9,11},{10,... | collective-permute-start | bytes 61448 | tf_op jit(solution)/shard_map/ppermute | solution.py:37
  98.6 5.8 %collective-permute-start.50 = (f32[40,128]{1,0:T(8,128)S(1)}, f32[40,128]{1,0:T(8,128)S(1)}, u32[]{:S(2)}, u32[]{:S(2)}) collective-permute-start(f32[40,128]{1,0:T(8,128)S(1)} %add_add_fusion.refs_0_), channel_id=1, source_target_pairs={{0,24},{8,16},{16,8},{24,0},{1,25},{9,17},{17,9},{25,1},{2,26},{10... | collective-permute-start | bytes 61448 | tf_op jit(solution)/shard_map/ppermute | solution.py:37
  101.2 4.7 %collective-permute-start.49 = (f32[40,128]{1,0:T(8,128)S(1)}, f32[40,128]{1,0:T(8,128)S(1)}, u32[]{:S(2)}, u32[]{:S(2)}) collective-permute-start(f32[40,128]{1,0:T(8,128)S(1)} %add_add_fusion.refs_0_), channel_id=1, source_target_pairs={{0,16},{8,24},{16,0},{24,8},{1,17},{9,25},{17,1},{25,9},{2,18},{10... | collective-permute-start | bytes 61448 | tf_op jit(solution)/shard_map/ppermute | solution.py:37
  101.2 4.7 %collective-permute-start.48 = (f32[40,128]{1,0:T(8,128)S(1)}, f32[40,128]{1,0:T(8,128)S(1)}, u32[]{:S(2)}, u32[]{:S(2)}) collective-permute-start(f32[40,128]{1,0:T(8,128)S(1)} %add_add_fusion.refs_0_), channel_id=1, source_target_pairs={{0,8},{8,0},{16,24},{24,16},{1,9},{9,1},{17,25},{25,17},{2,10},{10... | collective-permute-start | bytes 61448 | tf_op jit(solution)/shard_map/ppermute | solution.py:37
  (9 other events, 29.5 us)

commit v9 on v8

--- a/solution.py
+++ b/solution.py
@@ -324,7 +324,7 @@
         col_runs += [[(d * group, cut)], [(d * group + cut, late), *passed]]
     row_runs = [[((2 * d + core) * group, group)] for core in range(2) for d in range(chips_n)]
     runs = (col_runs, row_runs)
-    order = [*range(rows_n // 2, rows_n), *range(1, rows_n // 2)]
+    order = [*range(1, rows_n)]
 
     def gather(rounded, first=()):
         held = [rounded]
@@ -341,7 +341,7 @@
 
     def apply(rounded, degree=()):
         kept, swap, col_own, col_send = products(
-            tiles, table, *gather(rounded, degree), runs, order, degree
+            tiles, table, *gather(rounded), runs, order, degree
         )
         col_got = [trade(part, "row", d) for d, part in zip(order, col_send)]
         row_own, *row_send = merge(kept, trade(swap, "col", 1), degree)

time: 113 us -> 107 us (0.947)
  waiting for transfers between devices: 39.7 us -> 30 us
  starting transfers between devices: 53.2 us -> 57.7 us
    ppermute x51, waiting for transfers between devices: 39.7 us -> 30 us  [trade(): return lax.ppermute(part, axis, [(i, i ^ d) for i in range(n)])]
    ppermute x51, starting transfers between devices: 53.2 us -> 57.7 us  [trade(): return lax.ppermute(part, axis, [(i, i ^ d) for i in range(n)])]
  transfers between devices with their start and end apart: 51 -> 51, of which waited for: 26 -> 24; matrix products, arithmetic and copies ran while one was open for 0% -> 0% of each run, Pallas kernels for 2% -> 2%
where the time goes in v9:
time: 107 us
  starting transfers between devices  57.7 us (54%)
  waiting for transfers between devices  30 us (28%)
  Pallas kernels  15.7 us (15%)
  local copies, waits for them, and re-layouts  2.87 us (3%)
    ppermute x51, starting transfers between devices, trade(): return lax.ppermute(part, axis, [(i, i ^ d) for i in range(n)])  57.7 us
    ppermute x51, waiting for transfers between devices, trade(): return lax.ppermute(part, axis, [(i, i ^ d) for i in range(n)])  30 us
    pallas_call x10, Pallas kernels, call(): pl.pallas_call(kernel, out_shape=out_shape, in_specs=[SMEM] * smem + [VME...  15.7 us
    unnamed x12, local copies, waits for them, and re-layouts  2.83 us
  transfers between devices with their start and end apart: 51, of which 24 were waited for; matrix products, arithmetic and copies ran while one was open for 0% of the time, Pallas kernels for 2%

profile of v9, /device:TPU:0, one launch (start us, length us, event | category | flops | bytes accessed | tf_op | source)
XLA Modules:
  0.0 107.2 jit_solution(8131131975646855754)
XLA Ops:
  0.6 0.9 copy-done.2
  1.6 4.0 %collective-permute-start.5 = (bf16[8,64,128]{2,1,0:T(8,128)(2,1)S(1)}, bf16[8,64,128]{2,1,0:T(8,128)(2,1)S(1)}, u32[]{:S(2)}, u32[]{:S(2)}) collective-permute-start(bf16[8,64,128]{2,1,0:T(8,128)(2,1)S(1)} %shard_map.59.refs_0_.refs_4_), channel_id=1, source_target_pairs={{0,6},{1,7},{2,4},{3,5},{4,2},{5,3},{6,0},{7,1},{8,14},{9,15},{10,... | collective-permute-start | bytes 393224 | tf_op jit(solution)/shard_map/ppermute | solution.py:37
  6.2 3.0 %collective-permute-start.1 = (bf16[8,64,128]{2,1,0:T(8,128)(2,1)S(1)}, bf16[8,64,128]{2,1,0:T(8,128)(2,1)S(1)}, u32[]{:S(2)}, u32[]{:S(2)}) collective-permute-start(bf16[8,64,128]{2,1,0:T(8,128)(2,1)S(1)} %shard_map.59.refs_0_.refs_4_), channel_id=1, source_target_pairs={{0,16},{8,24},{16,0},{24,8},{1,17},{9,25},{17,1},{25,9},{2,18},{10... | collective-permute-start | bytes 393224 | tf_op jit(solution)/shard_map/ppermute | solution.py:37
  9.2 1.6 %collective-permute-start = (bf16[7,64,128]{2,1,0:T(8,128)(2,1)S(1)}, bf16[7,64,128]{2,1,0:T(8,128)(2,1)S(1)}, u32[]{:S(2)}, u32[]{:S(2)}) collective-permute-start(bf16[7,64,128]{2,1,0:T(8,128)(2,1)S(1)} %slice.24), channel_id=1, source_target_pairs={{0,8},{8,0},{16,24},{24,16},{1,9},{9,1},{17,25},{25,17},{2,10},{10... | collective-permute-start | bytes 344072 | tf_op jit(solution)/shard_map/ppermute | solution.py:37
  11.6 3.3 %collective-permute-done.refs_2_ = bf16[7,64,128]{2,1,0:T(8,128)(2,1)S(1)} collective-permute-done((bf16[7,64,128]{2,1,0:T(8,128)(2,1)S(1)}, bf16[7,64,128]{2,1,0:T(8,128)(2,1)S(1)}, u32[]{:S(2)}, u32[]{:S(2)}) %collective-permute-start) | collective-permute-done | bytes 114720 | tf_op jit(solution)/shard_map/ppermute | solution.py:37
  14.9 1.3 %collective-permute-start.2 = (bf16[9,64,128]{2,1,0:T(8,128)(2,1)S(1)}, bf16[9,64,128]{2,1,0:T(8,128)(2,1)S(1)}, u32[]{:S(2)}, u32[]{:S(2)}) collective-permute-start(bf16[9,64,128]{2,1,0:T(8,128)(2,1)S(1)} %pad_maximum_fusion), channel_id=1, source_target_pairs={{0,8},{8,0},{16,24},{24,16},{1,9},{9,1},{17,25},{25,17},{2,10},{10... | collective-permute-start | bytes 442376 | tf_op jit(solution)/shard_map/ppermute | solution.py:37
  16.9 1.2 %copy-done = bf16[1,1,32,128,128]{4,3,2,1,0:T(8,128)(2,1)S(1)} copy-done((bf16[1,1,32,128,128]{4,3,2,1,0:T(8,128)(2,1)S(1)}, bf16[1,1,32,128,128]{4,3,2,1,0:T(8,128)(2,1)}, u32[]{:S(2)}) %copy-start) | copy-done | bytes 1048600
  18.2 1.5 %shard_map.60 = (f32[64,128]{1,0:T(8,128)S(1)}, f32[32,128]{1,0:T(8,128)S(1)}) custom-call(s32[3,32]{1,0:T(4,128)S(1)} %fusion.1.table, bf16[32,128,128]{2,1,0:T(8,128)(2,1)S(1)} %bitcast.6), custom_call_target="tpu_custom_call" | custom-call | flops 33554432 | bytes 1048960 | tf_op jit(solution)/shard_map/pallas_call | solution.py:24
  19.7 1.4 %collective-permute-done.2.refs_3_ = bf16[9,64,128]{2,1,0:T(8,128)(2,1)S(1)} collective-permute-done((bf16[9,64,128]{2,1,0:T(8,128)(2,1)S(1)}, bf16[9,64,128]{2,1,0:T(8,128)(2,1)S(1)}, u32[]{:S(2)}, u32[]{:S(2)}) %collective-permute-start.2) | collective-permute-done | bytes 147488 | tf_op jit(solution)/shard_map/ppermute | solution.py:37
  21.2 1.9 %shard_map.61 = (f32[4,8,64,128]{3,2,1,0:T(8,128)S(1)}, bf16[4,528,128]{2,1,0:T(8,128)(2,1)S(1)}, f32[8,64,128]{2,1,0:T(8,128)S(1)}, bf16[528,128]{1,0:T(8,128)(...) custom-call(s32[3,32]{1,0:T(4,128)S(1)} %fusion.1.table, bf16[32,128,128]{2,1,0:T(8,128)(2,1)S(1)} %bitcast.7, ...), custom_call_target="tpu_custom_call" | custom-call | flops 134217728 | bytes 2670976 | tf_op jit(solution)/shard_map/pallas_call | solution.py:24
  23.2 1.3 %collective-permute-start.14 = (bf16[528,128]{1,0:T(8,128)(2,1)S(1)}, bf16[528,128]{1,0:T(8,128)(2,1)S(1)}, u32[]{:S(2)}, u32[]{:S(2)}) collective-permute-start(bf16[528,128]{1,0:T(8,128)(2,1)S(1)} %get-tuple-element.49), channel_id=1, source_target_pairs={{0,8},{8,0},{16,24},{24,16},{1,9},{9,1},{17,25},{25,17},{2,10},{10... | collective-permute-start | bytes 405512 | tf_op jit(solution)/shard_map/ppermute | solution.py:37
  24.4 1.6 %collective-permute-start.15 = (bf16[528,128]{1,0:T(8,128)(2,1)S(1)}, bf16[528,128]{1,0:T(8,128)(2,1)S(1)}, u32[]{:S(2)}, u32[]{:S(2)}) collective-permute-start(bf16[528,128]{1,0:T(8,128)(2,1)S(1)} %get-tuple-element.50), channel_id=1, source_target_pairs={{0,16},{8,24},{16,0},{24,8},{1,17},{9,25},{17,1},{25,9},{2,18},{10... | collective-permute-start | bytes 405512 | tf_op jit(solution)/shard_map/ppermute | solution.py:37
  26.0 1.6 %collective-permute-start.16 = (bf16[528,128]{1,0:T(8,128)(2,1)S(1)}, bf16[528,128]{1,0:T(8,128)(2,1)S(1)}, u32[]{:S(2)}, u32[]{:S(2)}) collective-permute-start(bf16[528,128]{1,0:T(8,128)(2,1)S(1)} %get-tuple-element.51), channel_id=1, source_target_pairs={{0,24},{8,16},{16,8},{24,0},{1,25},{9,17},{17,9},{25,1},{2,26},{10... | collective-permute-start | bytes 405512 | tf_op jit(solution)/shard_map/ppermute | solution.py:37
  27.7 1.6 %collective-permute-start.11 = (bf16[528,128]{1,0:T(8,128)(2,1)S(1)}, bf16[528,128]{1,0:T(8,128)(2,1)S(1)}, u32[]{:S(2)}, u32[]{:S(2)}) collective-permute-start(bf16[528,128]{1,0:T(8,128)(2,1)S(1)} %get-tuple-element.46), channel_id=1, source_target_pairs={{0,2},{1,3},{2,0},{3,1},{4,6},{5,7},{6,4},{7,5},{8,10},{9,11},{10,... | collective-permute-start | bytes 405512 | tf_op jit(solution)/shard_map/ppermute | solution.py:37
  29.3 1.5 %collective-permute-start.12 = (bf16[528,128]{1,0:T(8,128)(2,1)S(1)}, bf16[528,128]{1,0:T(8,128)(2,1)S(1)}, u32[]{:S(2)}, u32[]{:S(2)}) collective-permute-start(bf16[528,128]{1,0:T(8,128)(2,1)S(1)} %get-tuple-element.47), channel_id=1, source_target_pairs={{0,4},{1,5},{2,6},{3,7},{4,0},{5,1},{6,2},{7,3},{8,12},{9,13},{10,... | collective-permute-start | bytes 405512 | tf_op jit(solution)/shard_map/ppermute | solution.py:37
  30.9 2.5 %collective-permute-start.13 = (bf16[528,128]{1,0:T(8,128)(2,1)S(1)}, bf16[528,128]{1,0:T(8,128)(2,1)S(1)}, u32[]{:S(2)}, u32[]{:S(2)}) collective-permute-start(bf16[528,128]{1,0:T(8,128)(2,1)S(1)} %get-tuple-element.48), channel_id=1, source_target_pairs={{0,6},{1,7},{2,4},{3,5},{4,2},{5,3},{6,0},{7,1},{8,14},{9,15},{10,... | collective-permute-start | bytes 405512 | tf_op jit(solution)/shard_map/ppermute | solution.py:37
  33.4 4.2 %collective-permute-done.15.refs_4_ = bf16[528,128]{1,0:T(8,128)(2,1)S(1)} collective-permute-done((bf16[528,128]{1,0:T(8,128)(2,1)S(1)}, bf16[528,128]{1,0:T(8,128)(2,1)S(1)}, u32[]{:S(2)}, u32[]{:S(2)}) %collective-permute-start.15) | collective-permute-done | bytes 135200 | tf_op jit(solution)/shard_map/ppermute | solution.py:37
  37.8 2.7 %collective-permute-start.18 = (bf16[8,64,128]{2,1,0:T(8,128)(2,1)S(1)}, bf16[8,64,128]{2,1,0:T(8,128)(2,1)S(1)}, u32[]{:S(2)}, u32[]{:S(2)}) collective-permute-start(bf16[8,64,128]{2,1,0:T(8,128)(2,1)S(1)} %get-tuple-element.54.refs_0_.refs_4_), channel_id=1, source_target_pairs={{0,16},{8,24},{16,0},{24,8},{1,17},{9,25},{17,1},{25,9},{2,18},{10... | collective-permute-start | bytes 393224 | tf_op jit(solution)/shard_map/ppermute | solution.py:37
  40.6 2.5 %collective-permute-start.22 = (bf16[8,64,128]{2,1,0:T(8,128)(2,1)S(1)}, bf16[8,64,128]{2,1,0:T(8,128)(2,1)S(1)}, u32[]{:S(2)}, u32[]{:S(2)}) collective-permute-start(bf16[8,64,128]{2,1,0:T(8,128)(2,1)S(1)} %get-tuple-element.54.refs_0_.refs_4_), channel_id=1, source_target_pairs={{0,6},{1,7},{2,4},{3,5},{4,2},{5,3},{6,0},{7,1},{8,14},{9,15},{10,... | collective-permute-start | bytes 393224 | tf_op jit(solution)/shard_map/ppermute | solution.py:37
  44.2 2.0 %collective-permute-done.17.refs_2_ = bf16[7,64,128]{2,1,0:T(8,128)(2,1)S(1)} collective-permute-done((bf16[7,64,128]{2,1,0:T(8,128)(2,1)S(1)}, bf16[7,64,128]{2,1,0:T(8,128)(2,1)S(1)}, u32[]{:S(2)}, u32[]{:S(2)}) %collective-permute-start.17) | collective-permute-done | bytes 114720 | tf_op jit(solution)/shard_map/ppermute | solution.py:37
  46.2 1.3 %collective-permute-start.19 = (bf16[9,64,128]{2,1,0:T(8,128)(2,1)S(1)}, bf16[9,64,128]{2,1,0:T(8,128)(2,1)S(1)}, u32[]{:S(2)}, u32[]{:S(2)}) collective-permute-start(bf16[9,64,128]{2,1,0:T(8,128)(2,1)S(1)} %pad_maximum_fusion.1), channel_id=1, source_target_pairs={{0,8},{8,0},{16,24},{24,16},{1,9},{9,1},{17,25},{25,17},{2,10},{10... | collective-permute-start | bytes 442376 | tf_op jit(solution)/shard_map/ppermute | solution.py:37
  49.3 0.8 collective-permute-done.25.refs_10_
  50.3 1.1 collective-permute-done.19.refs_3_
  51.4 1.9 %shard_map.64 = (f32[4,8,64,128]{3,2,1,0:T(8,128)S(1)}, bf16[4,512,128]{2,1,0:T(8,128)(2,1)S(1)}, f32[8,64,128]{2,1,0:T(8,128)S(1)}, bf16[512,128]{1,0:T(8,128)(...) custom-call(s32[3,32]{1,0:T(4,128)S(1)} %fusion.1.table, bf16[32,128,128]{2,1,0:T(8,128)(2,1)S(1)} %bitcast.8, ...), custom_call_target="tpu_custom_call" | custom-call | flops 134217728 | bytes 2621824 | tf_op jit(solution)/shard_map/pallas_call | solution.py:24
  53.4 1.3 %collective-permute-start.31 = (bf16[512,128]{1,0:T(8,128)(2,1)S(1)}, bf16[512,128]{1,0:T(8,128)(2,1)S(1)}, u32[]{:S(2)}, u32[]{:S(2)}) collective-permute-start(bf16[512,128]{1,0:T(8,128)(2,1)S(1)} %get-tuple-element.64), channel_id=1, source_target_pairs={{0,8},{8,0},{16,24},{24,16},{1,9},{9,1},{17,25},{25,17},{2,10},{10... | collective-permute-start | bytes 393224 | tf_op jit(solution)/shard_map/ppermute | solution.py:37
  54.7 2.1 %collective-permute-start.32 = (bf16[512,128]{1,0:T(8,128)(2,1)S(1)}, bf16[512,128]{1,0:T(8,128)(2,1)S(1)}, u32[]{:S(2)}, u32[]{:S(2)}) collective-permute-start(bf16[512,128]{1,0:T(8,128)(2,1)S(1)} %get-tuple-element.65), channel_id=1, source_target_pairs={{0,16},{8,24},{16,0},{24,8},{1,17},{9,25},{17,1},{25,9},{2,18},{10... | collective-permute-start | bytes 393224 | tf_op jit(solution)/shard_map/ppermute | solution.py:37
  56.8 1.0 collective-permute-start.33
  57.9 1.6 %collective-permute-start.28 = (bf16[512,128]{1,0:T(8,128)(2,1)S(1)}, bf16[512,128]{1,0:T(8,128)(2,1)S(1)}, u32[]{:S(2)}, u32[]{:S(2)}) collective-permute-start(bf16[512,128]{1,0:T(8,128)(2,1)S(1)} %get-tuple-element.61), channel_id=1, source_target_pairs={{0,2},{1,3},{2,0},{3,1},{4,6},{5,7},{6,4},{7,5},{8,10},{9,11},{10,... | collective-permute-start | bytes 393224 | tf_op jit(solution)/shard_map/ppermute | solution.py:37
  59.5 1.5 %collective-permute-start.29 = (bf16[512,128]{1,0:T(8,128)(2,1)S(1)}, bf16[512,128]{1,0:T(8,128)(2,1)S(1)}, u32[]{:S(2)}, u32[]{:S(2)}) collective-permute-start(bf16[512,128]{1,0:T(8,128)(2,1)S(1)} %get-tuple-element.62), channel_id=1, source_target_pairs={{0,4},{1,5},{2,6},{3,7},{4,0},{5,1},{6,2},{7,3},{8,12},{9,13},{10,... | collective-permute-start | bytes 393224 | tf_op jit(solution)/shard_map/ppermute | solution.py:37
  61.7 2.4 %collective-permute-start.30 = (bf16[512,128]{1,0:T(8,128)(2,1)S(1)}, bf16[512,128]{1,0:T(8,128)(2,1)S(1)}, u32[]{:S(2)}, u32[]{:S(2)}) collective-permute-start(bf16[512,128]{1,0:T(8,128)(2,1)S(1)} %get-tuple-element.63), channel_id=1, source_target_pairs={{0,6},{1,7},{2,4},{3,5},{4,2},{5,3},{6,0},{7,1},{8,14},{9,15},{10,... | collective-permute-start | bytes 393224 | tf_op jit(solution)/shard_map/ppermute | solution.py:37
  64.2 3.5 %collective-permute-done.32.refs_4_ = bf16[512,128]{1,0:T(8,128)(2,1)S(1)} collective-permute-done((bf16[512,128]{1,0:T(8,128)(2,1)S(1)}, bf16[512,128]{1,0:T(8,128)(2,1)S(1)}, u32[]{:S(2)}, u32[]{:S(2)}) %collective-permute-start.32) | collective-permute-done | bytes 131104 | tf_op jit(solution)/shard_map/ppermute | solution.py:37
  67.7 0.8 shard_map.66
  68.4 3.8 %collective-permute-start.35 = (bf16[8,64,128]{2,1,0:T(8,128)(2,1)S(1)}, bf16[8,64,128]{2,1,0:T(8,128)(2,1)S(1)}, u32[]{:S(2)}, u32[]{:S(2)}) collective-permute-start(bf16[8,64,128]{2,1,0:T(8,128)(2,1)S(1)} %get-tuple-element.69.refs_0_.refs_4_), channel_id=1, source_target_pairs={{0,16},{8,24},{16,0},{24,8},{1,17},{9,25},{17,1},{25,9},{2,18},{10... | collective-permute-start | bytes 393224 | tf_op jit(solution)/shard_map/ppermute | solution.py:37
  72.4 2.5 %collective-permute-start.39 = (bf16[8,64,128]{2,1,0:T(8,128)(2,1)S(1)}, bf16[8,64,128]{2,1,0:T(8,128)(2,1)S(1)}, u32[]{:S(2)}, u32[]{:S(2)}) collective-permute-start(bf16[8,64,128]{2,1,0:T(8,128)(2,1)S(1)} %get-tuple-element.69.refs_0_.refs_4_), channel_id=1, source_target_pairs={{0,6},{1,7},{2,4},{3,5},{4,2},{5,3},{6,0},{7,1},{8,14},{9,15},{10,... | collective-permute-start | bytes 393224 | tf_op jit(solution)/shard_map/ppermute | solution.py:37
  75.9 2.4 %collective-permute-done.34.refs_2_ = bf16[7,64,128]{2,1,0:T(8,128)(2,1)S(1)} collective-permute-done((bf16[7,64,128]{2,1,0:T(8,128)(2,1)S(1)}, bf16[7,64,128]{2,1,0:T(8,128)(2,1)S(1)}, u32[]{:S(2)}, u32[]{:S(2)}) %collective-permute-start.34) | collective-permute-done | bytes 114720 | tf_op jit(solution)/shard_map/ppermute | solution.py:37
  78.3 1.2 %collective-permute-start.36 = (bf16[9,64,128]{2,1,0:T(8,128)(2,1)S(1)}, bf16[9,64,128]{2,1,0:T(8,128)(2,1)S(1)}, u32[]{:S(2)}, u32[]{:S(2)}) collective-permute-start(bf16[9,64,128]{2,1,0:T(8,128)(2,1)S(1)} %pad_maximum_fusion.2), channel_id=1, source_target_pairs={{0,8},{8,0},{16,24},{24,16},{1,9},{9,1},{17,25},{25,17},{2,10},{10... | collective-permute-start | bytes 442376 | tf_op jit(solution)/shard_map/ppermute | solution.py:37
  81.1 0.8 collective-permute-done.42.refs_10_
  82.1 1.4 %collective-permute-done.36.refs_3_ = bf16[9,64,128]{2,1,0:T(8,128)(2,1)S(1)} collective-permute-done((bf16[9,64,128]{2,1,0:T(8,128)(2,1)S(1)}, bf16[9,64,128]{2,1,0:T(8,128)(2,1)S(1)}, u32[]{:S(2)}, u32[]{:S(2)}) %collective-permute-start.36) | collective-permute-done | bytes 147488 | tf_op jit(solution)/shard_map/ppermute | solution.py:37
  83.5 2.0 %shard_map.67 = f32[40,128]{1,0:T(8,128)S(1)} custom-call(s32[3,32]{1,0:T(4,128)S(1)} %fusion.1.table, bf16[32,128,128]{2,1,0:T(8,128)(2,1)S(1)} %bitcast.9, f32[64,128]{1,0:T(8,128)S(1)} %get-tuple-element.68.gram_ref, bf16[8,64,128]{2,1,0:T(8,128)(2,1)S(1)} %get-tuple-element.69.refs_0_.refs_4_, bf16[8,64,128]{2,1,0:T(8,128)(2,1)S(1)} %collective-permute-done.35.refs_1_, ...), custom_call_target="tpu_custom_call" | custom-call | flops 134217728 | bytes 2654592 | tf_op jit(solution)/shard_map/pallas_call | solution.py:24
  85.6 1.2 %collective-permute-done.44 = f32[40,128]{1,0:T(8,128)S(1)} collective-permute-done((f32[40,128]{1,0:T(8,128)S(1)}, f32[40,128]{1,0:T(8,128)S(1)}, u32[]{:S(2)}, u32[]{:S(2)}) %collective-permute-start.44) | collective-permute-done | bytes 20512 | tf_op jit(solution)/shard_map/ppermute | solution.py:37
  86.8 2.5 %collective-permute-start.47 = (f32[40,128]{1,0:T(8,128)S(1)}, f32[40,128]{1,0:T(8,128)S(1)}, u32[]{:S(2)}, u32[]{:S(2)}) collective-permute-start(f32[40,128]{1,0:T(8,128)S(1)} %add.76), channel_id=1, source_target_pairs={{0,6},{1,7},{2,4},{3,5},{4,2},{5,3},{6,0},{7,1},{8,14},{9,15},{10,... | collective-permute-start | bytes 61448 | tf_op jit(solution)/shard_map/ppermute | solution.py:37
  90.3 1.2 %collective-permute-done.47 = f32[40,128]{1,0:T(8,128)S(1)} collective-permute-done((f32[40,128]{1,0:T(8,128)S(1)}, f32[40,128]{1,0:T(8,128)S(1)}, u32[]{:S(2)}, u32[]{:S(2)}) %collective-permute-start.47) | collective-permute-done | bytes 20512 | tf_op jit(solution)/shard_map/ppermute | solution.py:37
  91.5 1.6 %collective-permute-done.46 = f32[40,128]{1,0:T(8,128)S(1)} collective-permute-done((f32[40,128]{1,0:T(8,128)S(1)}, f32[40,128]{1,0:T(8,128)S(1)}, u32[]{:S(2)}, u32[]{:S(2)}) %collective-permute-start.46) | collective-permute-done | bytes 20512 | tf_op jit(solution)/shard_map/ppermute | solution.py:37
  93.5 0.9 collective-permute-start.50
  94.5 1.8 %collective-permute-start.49 = (f32[40,128]{1,0:T(8,128)S(1)}, f32[40,128]{1,0:T(8,128)S(1)}, u32[]{:S(2)}, u32[]{:S(2)}) collective-permute-start(f32[40,128]{1,0:T(8,128)S(1)} %add_add_fusion.refs_0_), channel_id=1, source_target_pairs={{0,16},{8,24},{16,0},{24,8},{1,17},{9,25},{17,1},{25,9},{2,18},{10... | collective-permute-start | bytes 61448 | tf_op jit(solution)/shard_map/ppermute | solution.py:37
  96.2 1.7 %collective-permute-start.48 = (f32[40,128]{1,0:T(8,128)S(1)}, f32[40,128]{1,0:T(8,128)S(1)}, u32[]{:S(2)}, u32[]{:S(2)}) collective-permute-start(f32[40,128]{1,0:T(8,128)S(1)} %add_add_fusion.refs_0_), channel_id=1, source_target_pairs={{0,8},{8,0},{16,24},{24,16},{1,9},{9,1},{17,25},{25,17},{2,10},{10... | collective-permute-start | bytes 61448 | tf_op jit(solution)/shard_map/ppermute | solution.py:37
  98.0 1.3 %collective-permute-done.50.refs_3_ = f32[40,128]{1,0:T(8,128)S(1)} collective-permute-done((f32[40,128]{1,0:T(8,128)S(1)}, f32[40,128]{1,0:T(8,128)S(1)}, u32[]{:S(2)}, u32[]{:S(2)}) %collective-permute-start.50) | collective-permute-done | bytes 20512 | tf_op jit(solution)/shard_map/ppermute | solution.py:37
  100.0 7.2 %shard_map.68 = (f32[64,1024]{1,0:T(8,128)}, f32[64,64]{1,0:T(8,128)}) custom-call(f32[64,1024]{1,0:T(8,128)S(1)} %get-tuple-element.67.filtered_ref, f32[40,128]{1,0:T(8,128)S(1)} %add_add_fusion.refs_0_, f32[40,128]{1,0:T(8,128)S(1)} %collective-permute-done.48.refs_1_, f32[40,128]{1,0:T(8,128)S(1)} %collective-permute-done.49.refs_2_, ...), custom_call_target="tpu_custom_call" | custom-call | bytes 344064 | tf_op jit(solution)/shard_map/pallas_call | solution.py:24
  (90 shorter events, 11.8 us)
Async XLA Ops:
  1.6 14.5 %collective-permute-start.5 = (bf16[8,64,128]{2,1,0:T(8,128)(2,1)S(1)}, bf16[8,64,128]{2,1,0:T(8,128)(2,1)S(1)}, u32[]{:S(2)}, u32[]{:S(2)}) collective-permute-start(bf16[8,64,128]{2,1,0:T(8,128)(2,1)S(1)} %shard_map.59.refs_0_.refs_4_), channel_id=1, source_target_pairs={{0,6},{1,7},{2,4},{3,5},{4,2},{5,3},{6,0},{7,1},{8,14},{9,15},{10,... | collective-permute-start | bytes 393224 | tf_op jit(solution)/shard_map/ppermute | solution.py:37
  5.6 10.8 %collective-permute-start.4 = (bf16[8,64,128]{2,1,0:T(8,128)(2,1)S(1)}, bf16[8,64,128]{2,1,0:T(8,128)(2,1)S(1)}, u32[]{:S(2)}, u32[]{:S(2)}) collective-permute-start(bf16[8,64,128]{2,1,0:T(8,128)(2,1)S(1)} %shard_map.59.refs_0_.refs_4_), channel_id=1, source_target_pairs={{0,4},{1,5},{2,6},{3,7},{4,0},{5,1},{6,2},{7,3},{8,12},{9,13},{10,... | collective-permute-start | bytes 393224 | tf_op jit(solution)/shard_map/ppermute | solution.py:37
  6.1 10.6 %collective-permute-start.3 = (bf16[8,64,128]{2,1,0:T(8,128)(2,1)S(1)}, bf16[8,64,128]{2,1,0:T(8,128)(2,1)S(1)}, u32[]{:S(2)}, u32[]{:S(2)}) collective-permute-start(bf16[8,64,128]{2,1,0:T(8,128)(2,1)S(1)} %shard_map.59.refs_0_.refs_4_), channel_id=1, source_target_pairs={{0,2},{1,3},{2,0},{3,1},{4,6},{5,7},{6,4},{7,5},{8,10},{9,11},{10,... | collective-permute-start | bytes 393224 | tf_op jit(solution)/shard_map/ppermute | solution.py:37
  6.2 8.6 %collective-permute-start.1 = (bf16[8,64,128]{2,1,0:T(8,128)(2,1)S(1)}, bf16[8,64,128]{2,1,0:T(8,128)(2,1)S(1)}, u32[]{:S(2)}, u32[]{:S(2)}) collective-permute-start(bf16[8,64,128]{2,1,0:T(8,128)(2,1)S(1)} %shard_map.59.refs_0_.refs_4_), channel_id=1, source_target_pairs={{0,16},{8,24},{16,0},{24,8},{1,17},{9,25},{17,1},{25,9},{2,18},{10... | collective-permute-start | bytes 393224 | tf_op jit(solution)/shard_map/ppermute | solution.py:37
  9.2 5.6 %collective-permute-start = (bf16[7,64,128]{2,1,0:T(8,128)(2,1)S(1)}, bf16[7,64,128]{2,1,0:T(8,128)(2,1)S(1)}, u32[]{:S(2)}, u32[]{:S(2)}) collective-permute-start(bf16[7,64,128]{2,1,0:T(8,128)(2,1)S(1)} %slice.24), channel_id=1, source_target_pairs={{0,8},{8,0},{16,24},{24,16},{1,9},{9,1},{17,25},{25,17},{2,10},{10... | collective-permute-start | bytes 344072 | tf_op jit(solution)/shard_map/ppermute | solution.py:37
  14.8 4.9 %collective-permute-start.6 = (bf16[8,64,128]{2,1,0:T(8,128)(2,1)S(1)}, bf16[8,64,128]{2,1,0:T(8,128)(2,1)S(1)}, u32[]{:S(2)}, u32[]{:S(2)}) collective-permute-start(bf16[8,64,128]{2,1,0:T(8,128)(2,1)S(1)} %shard_map.59.refs_0_.refs_4_), channel_id=1, source_target_pairs={{0,1},{1,0},{2,3},{3,2},{4,5},{5,4},{6,7},{7,6},{8,9},{9,8},{10,11... | collective-permute-start | bytes 393224 | tf_op jit(solution)/shard_map/ppermute | solution.py:37
  14.9 6.3 %collective-permute-start.2 = (bf16[9,64,128]{2,1,0:T(8,128)(2,1)S(1)}, bf16[9,64,128]{2,1,0:T(8,128)(2,1)S(1)}, u32[]{:S(2)}, u32[]{:S(2)}) collective-permute-start(bf16[9,64,128]{2,1,0:T(8,128)(2,1)S(1)} %pad_maximum_fusion), channel_id=1, source_target_pairs={{0,8},{8,0},{16,24},{24,16},{1,9},{9,1},{17,25},{25,17},{2,10},{10... | collective-permute-start | bytes 442376 | tf_op jit(solution)/shard_map/ppermute | solution.py:37
  16.1 3.6 %collective-permute-start.9 = (bf16[8,64,128]{2,1,0:T(8,128)(2,1)S(1)}, bf16[8,64,128]{2,1,0:T(8,128)(2,1)S(1)}, u32[]{:S(2)}, u32[]{:S(2)}) collective-permute-start(bf16[8,64,128]{2,1,0:T(8,128)(2,1)S(1)} %collective-permute-done.5.refs_7_), channel_id=1, source_target_pairs={{0,1},{1,0},{2,3},{3,2},{4,5},{5,4},{6,7},{7,6},{8,9},{9,8},{10,11... | collective-permute-start | bytes 393224 | tf_op jit(solution)/shard_map/ppermute | solution.py:37
  16.4 3.3 %collective-permute-start.8 = (bf16[8,64,128]{2,1,0:T(8,128)(2,1)S(1)}, bf16[8,64,128]{2,1,0:T(8,128)(2,1)S(1)}, u32[]{:S(2)}, u32[]{:S(2)}) collective-permute-start(bf16[8,64,128]{2,1,0:T(8,128)(2,1)S(1)} %collective-permute-done.4.refs_6_), channel_id=1, source_target_pairs={{0,1},{1,0},{2,3},{3,2},{4,5},{5,4},{6,7},{7,6},{8,9},{9,8},{10,11... | collective-permute-start | bytes 393224 | tf_op jit(solution)/shard_map/ppermute | solution.py:37
  16.7 3.1 %collective-permute-start.7 = (bf16[8,64,128]{2,1,0:T(8,128)(2,1)S(1)}, bf16[8,64,128]{2,1,0:T(8,128)(2,1)S(1)}, u32[]{:S(2)}, u32[]{:S(2)}) collective-permute-start(bf16[8,64,128]{2,1,0:T(8,128)(2,1)S(1)} %collective-permute-done.3.refs_5_), channel_id=1, source_target_pairs={{0,1},{1,0},{2,3},{3,2},{4,5},{5,4},{6,7},{7,6},{8,9},{9,8},{10,11... | collective-permute-start | bytes 393224 | tf_op jit(solution)/shard_map/ppermute | solution.py:37
  23.1 4.5 %collective-permute-start.10 = (bf16[4,528,128]{2,1,0:T(8,128)(2,1)S(1)}, bf16[4,528,128]{2,1,0:T(8,128)(2,1)S(1)}, u32[]{:S(2)}, u32[]{:S(2)}) collective-permute-start(bf16[4,528,128]{2,1,0:T(8,128)(2,1)S(1)} %get-tuple-element.42), channel_id=1, source_target_pairs={{0,1},{1,0},{2,3},{3,2},{4,5},{5,4},{6,7},{7,6},{8,9},{9,8},{10,11... | collective-permute-start | bytes 1622024 | tf_op jit(solution)/shard_map/ppermute | solution.py:37
  23.2 7.7 %collective-permute-start.14 = (bf16[528,128]{1,0:T(8,128)(2,1)S(1)}, bf16[528,128]{1,0:T(8,128)(2,1)S(1)}, u32[]{:S(2)}, u32[]{:S(2)}) collective-permute-start(bf16[528,128]{1,0:T(8,128)(2,1)S(1)} %get-tuple-element.49), channel_id=1, source_target_pairs={{0,8},{8,0},{16,24},{24,16},{1,9},{9,1},{17,25},{25,17},{2,10},{10... | collective-permute-start | bytes 405512 | tf_op jit(solution)/shard_map/ppermute | solution.py:37
  24.4 13.1 %collective-permute-start.15 = (bf16[528,128]{1,0:T(8,128)(2,1)S(1)}, bf16[528,128]{1,0:T(8,128)(2,1)S(1)}, u32[]{:S(2)}, u32[]{:S(2)}) collective-permute-start(bf16[528,128]{1,0:T(8,128)(2,1)S(1)} %get-tuple-element.50), channel_id=1, source_target_pairs={{0,16},{8,24},{16,0},{24,8},{1,17},{9,25},{17,1},{25,9},{2,18},{10... | collective-permute-start | bytes 405512 | tf_op jit(solution)/shard_map/ppermute | solution.py:37
  26.0 11.5 %collective-permute-start.16 = (bf16[528,128]{1,0:T(8,128)(2,1)S(1)}, bf16[528,128]{1,0:T(8,128)(2,1)S(1)}, u32[]{:S(2)}, u32[]{:S(2)}) collective-permute-start(bf16[528,128]{1,0:T(8,128)(2,1)S(1)} %get-tuple-element.51), channel_id=1, source_target_pairs={{0,24},{8,16},{16,8},{24,0},{1,25},{9,17},{17,9},{25,1},{2,26},{10... | collective-permute-start | bytes 405512 | tf_op jit(solution)/shard_map/ppermute | solution.py:37
  27.7 9.8 %collective-permute-start.11 = (bf16[528,128]{1,0:T(8,128)(2,1)S(1)}, bf16[528,128]{1,0:T(8,128)(2,1)S(1)}, u32[]{:S(2)}, u32[]{:S(2)}) collective-permute-start(bf16[528,128]{1,0:T(8,128)(2,1)S(1)} %get-tuple-element.46), channel_id=1, source_target_pairs={{0,2},{1,3},{2,0},{3,1},{4,6},{5,7},{6,4},{7,5},{8,10},{9,11},{10,... | collective-permute-start | bytes 405512 | tf_op jit(solution)/shard_map/ppermute | solution.py:37
  29.3 8.2 %collective-permute-start.12 = (bf16[528,128]{1,0:T(8,128)(2,1)S(1)}, bf16[528,128]{1,0:T(8,128)(2,1)S(1)}, u32[]{:S(2)}, u32[]{:S(2)}) collective-permute-start(bf16[528,128]{1,0:T(8,128)(2,1)S(1)} %get-tuple-element.47), channel_id=1, source_target_pairs={{0,4},{1,5},{2,6},{3,7},{4,0},{5,1},{6,2},{7,3},{8,12},{9,13},{10,... | collective-permute-start | bytes 405512 | tf_op jit(solution)/shard_map/ppermute | solution.py:37
  30.9 6.7 %collective-permute-start.13 = (bf16[528,128]{1,0:T(8,128)(2,1)S(1)}, bf16[528,128]{1,0:T(8,128)(2,1)S(1)}, u32[]{:S(2)}, u32[]{:S(2)}) collective-permute-start(bf16[528,128]{1,0:T(8,128)(2,1)S(1)} %get-tuple-element.48), channel_id=1, source_target_pairs={{0,6},{1,7},{2,4},{3,5},{4,2},{5,3},{6,0},{7,1},{8,14},{9,15},{10,... | collective-permute-start | bytes 405512 | tf_op jit(solution)/shard_map/ppermute | solution.py:37
  37.8 8.4 %collective-permute-start.18 = (bf16[8,64,128]{2,1,0:T(8,128)(2,1)S(1)}, bf16[8,64,128]{2,1,0:T(8,128)(2,1)S(1)}, u32[]{:S(2)}, u32[]{:S(2)}) collective-permute-start(bf16[8,64,128]{2,1,0:T(8,128)(2,1)S(1)} %get-tuple-element.54.refs_0_.refs_4_), channel_id=1, source_target_pairs={{0,16},{8,24},{16,0},{24,8},{1,17},{9,25},{17,1},{25,9},{2,18},{10... | collective-permute-start | bytes 393224 | tf_op jit(solution)/shard_map/ppermute | solution.py:37
  40.5 5.7 %collective-permute-start.17 = (bf16[7,64,128]{2,1,0:T(8,128)(2,1)S(1)}, bf16[7,64,128]{2,1,0:T(8,128)(2,1)S(1)}, u32[]{:S(2)}, u32[]{:S(2)}) collective-permute-start(bf16[7,64,128]{2,1,0:T(8,128)(2,1)S(1)} %slice.20), channel_id=1, source_target_pairs={{0,8},{8,0},{16,24},{24,16},{1,9},{9,1},{17,25},{25,17},{2,10},{10... | collective-permute-start | bytes 344072 | tf_op jit(solution)/shard_map/ppermute | solution.py:37
  40.6 6.9 %collective-permute-start.22 = (bf16[8,64,128]{2,1,0:T(8,128)(2,1)S(1)}, bf16[8,64,128]{2,1,0:T(8,128)(2,1)S(1)}, u32[]{:S(2)}, u32[]{:S(2)}) collective-permute-start(bf16[8,64,128]{2,1,0:T(8,128)(2,1)S(1)} %get-tuple-element.54.refs_0_.refs_4_), channel_id=1, source_target_pairs={{0,6},{1,7},{2,4},{3,5},{4,2},{5,3},{6,0},{7,1},{8,14},{9,15},{10,... | collective-permute-start | bytes 393224 | tf_op jit(solution)/shard_map/ppermute | solution.py:37
  43.1 5.7 %collective-permute-start.21 = (bf16[8,64,128]{2,1,0:T(8,128)(2,1)S(1)}, bf16[8,64,128]{2,1,0:T(8,128)(2,1)S(1)}, u32[]{:S(2)}, u32[]{:S(2)}) collective-permute-start(bf16[8,64,128]{2,1,0:T(8,128)(2,1)S(1)} %get-tuple-element.54.refs_0_.refs_4_), channel_id=1, source_target_pairs={{0,4},{1,5},{2,6},{3,7},{4,0},{5,1},{6,2},{7,3},{8,12},{9,13},{10,... | collective-permute-start | bytes 393224 | tf_op jit(solution)/shard_map/ppermute | solution.py:37
  43.6 5.3 %collective-permute-start.20 = (bf16[8,64,128]{2,1,0:T(8,128)(2,1)S(1)}, bf16[8,64,128]{2,1,0:T(8,128)(2,1)S(1)}, u32[]{:S(2)}, u32[]{:S(2)}) collective-permute-start(bf16[8,64,128]{2,1,0:T(8,128)(2,1)S(1)} %get-tuple-element.54.refs_0_.refs_4_), channel_id=1, source_target_pairs={{0,2},{1,3},{2,0},{3,1},{4,6},{5,7},{6,4},{7,5},{8,10},{9,11},{10,... | collective-permute-start | bytes 393224 | tf_op jit(solution)/shard_map/ppermute | solution.py:37
  46.2 5.2 %collective-permute-start.19 = (bf16[9,64,128]{2,1,0:T(8,128)(2,1)S(1)}, bf16[9,64,128]{2,1,0:T(8,128)(2,1)S(1)}, u32[]{:S(2)}, u32[]{:S(2)}) collective-permute-start(bf16[9,64,128]{2,1,0:T(8,128)(2,1)S(1)} %pad_maximum_fusion.1), channel_id=1, source_target_pairs={{0,8},{8,0},{16,24},{24,16},{1,9},{9,1},{17,25},{25,17},{2,10},{10... | collective-permute-start | bytes 442376 | tf_op jit(solution)/shard_map/ppermute | solution.py:37
  47.5 1.8 %collective-permute-start.23 = (bf16[8,64,128]{2,1,0:T(8,128)(2,1)S(1)}, bf16[8,64,128]{2,1,0:T(8,128)(2,1)S(1)}, u32[]{:S(2)}, u32[]{:S(2)}) collective-permute-start(bf16[8,64,128]{2,1,0:T(8,128)(2,1)S(1)} %get-tuple-element.54.refs_0_.refs_4_), channel_id=1, source_target_pairs={{0,1},{1,0},{2,3},{3,2},{4,5},{5,4},{6,7},{7,6},{8,9},{9,8},{10,11... | collective-permute-start | bytes 393224 | tf_op jit(solution)/shard_map/ppermute | solution.py:37
  47.5 1.8 %collective-permute-start.26 = (bf16[8,64,128]{2,1,0:T(8,128)(2,1)S(1)}, bf16[8,64,128]{2,1,0:T(8,128)(2,1)S(1)}, u32[]{:S(2)}, u32[]{:S(2)}) collective-permute-start(bf16[8,64,128]{2,1,0:T(8,128)(2,1)S(1)} %collective-permute-done.22.refs_7_), channel_id=1, source_target_pairs={{0,1},{1,0},{2,3},{3,2},{4,5},{5,4},{6,7},{7,6},{8,9},{9,8},{10,11... | collective-permute-start | bytes 393224 | tf_op jit(solution)/shard_map/ppermute | solution.py:37
  48.9 1.4 %collective-permute-start.24 = (bf16[8,64,128]{2,1,0:T(8,128)(2,1)S(1)}, bf16[8,64,128]{2,1,0:T(8,128)(2,1)S(1)}, u32[]{:S(2)}, u32[]{:S(2)}) collective-permute-start(bf16[8,64,128]{2,1,0:T(8,128)(2,1)S(1)} %collective-permute-done.20.refs_5_), channel_id=1, source_target_pairs={{0,1},{1,0},{2,3},{3,2},{4,5},{5,4},{6,7},{7,6},{8,9},{9,8},{10,11... | collective-permute-start | bytes 393224 | tf_op jit(solution)/shard_map/ppermute | solution.py:37
  53.3 4.5 %collective-permute-start.27 = (bf16[4,512,128]{2,1,0:T(8,128)(2,1)S(1)}, bf16[4,512,128]{2,1,0:T(8,128)(2,1)S(1)}, u32[]{:S(2)}, u32[]{:S(2)}) collective-permute-start(bf16[4,512,128]{2,1,0:T(8,128)(2,1)S(1)} %get-tuple-element.58), channel_id=1, source_target_pairs={{0,1},{1,0},{2,3},{3,2},{4,5},{5,4},{6,7},{7,6},{8,9},{9,8},{10,11... | collective-permute-start | bytes 1572872 | tf_op jit(solution)/shard_map/ppermute | solution.py:37
  53.4 8.3 %collective-permute-start.31 = (bf16[512,128]{1,0:T(8,128)(2,1)S(1)}, bf16[512,128]{1,0:T(8,128)(2,1)S(1)}, u32[]{:S(2)}, u32[]{:S(2)}) collective-permute-start(bf16[512,128]{1,0:T(8,128)(2,1)S(1)} %get-tuple-element.64), channel_id=1, source_target_pairs={{0,8},{8,0},{16,24},{24,16},{1,9},{9,1},{17,25},{25,17},{2,10},{10... | collective-permute-start | bytes 393224 | tf_op jit(solution)/shard_map/ppermute | solution.py:37
  54.7 12.9 %collective-permute-start.32 = (bf16[512,128]{1,0:T(8,128)(2,1)S(1)}, bf16[512,128]{1,0:T(8,128)(2,1)S(1)}, u32[]{:S(2)}, u32[]{:S(2)}) collective-permute-start(bf16[512,128]{1,0:T(8,128)(2,1)S(1)} %get-tuple-element.65), channel_id=1, source_target_pairs={{0,16},{8,24},{16,0},{24,8},{1,17},{9,25},{17,1},{25,9},{2,18},{10... | collective-permute-start | bytes 393224 | tf_op jit(solution)/shard_map/ppermute | solution.py:37
  56.8 10.8 %collective-permute-start.33 = (bf16[512,128]{1,0:T(8,128)(2,1)S(1)}, bf16[512,128]{1,0:T(8,128)(2,1)S(1)}, u32[]{:S(2)}, u32[]{:S(2)}) collective-permute-start(bf16[512,128]{1,0:T(8,128)(2,1)S(1)} %get-tuple-element.66), channel_id=1, source_target_pairs={{0,24},{8,16},{16,8},{24,0},{1,25},{9,17},{17,9},{25,1},{2,26},{10... | collective-permute-start | bytes 393224 | tf_op jit(solution)/shard_map/ppermute | solution.py:37
  57.9 9.7 %collective-permute-start.28 = (bf16[512,128]{1,0:T(8,128)(2,1)S(1)}, bf16[512,128]{1,0:T(8,128)(2,1)S(1)}, u32[]{:S(2)}, u32[]{:S(2)}) collective-permute-start(bf16[512,128]{1,0:T(8,128)(2,1)S(1)} %get-tuple-element.61), channel_id=1, source_target_pairs={{0,2},{1,3},{2,0},{3,1},{4,6},{5,7},{6,4},{7,5},{8,10},{9,11},{10,... | collective-permute-start | bytes 393224 | tf_op jit(solution)/shard_map/ppermute | solution.py:37
  59.5 8.1 %collective-permute-start.29 = (bf16[512,128]{1,0:T(8,128)(2,1)S(1)}, bf16[512,128]{1,0:T(8,128)(2,1)S(1)}, u32[]{:S(2)}, u32[]{:S(2)}) collective-permute-start(bf16[512,128]{1,0:T(8,128)(2,1)S(1)} %get-tuple-element.62), channel_id=1, source_target_pairs={{0,4},{1,5},{2,6},{3,7},{4,0},{5,1},{6,2},{7,3},{8,12},{9,13},{10,... | collective-permute-start | bytes 393224 | tf_op jit(solution)/shard_map/ppermute | solution.py:37
  61.7 5.9 %collective-permute-start.30 = (bf16[512,128]{1,0:T(8,128)(2,1)S(1)}, bf16[512,128]{1,0:T(8,128)(2,1)S(1)}, u32[]{:S(2)}, u32[]{:S(2)}) collective-permute-start(bf16[512,128]{1,0:T(8,128)(2,1)S(1)} %get-tuple-element.63), channel_id=1, source_target_pairs={{0,6},{1,7},{2,4},{3,5},{4,2},{5,3},{6,0},{7,1},{8,14},{9,15},{10,... | collective-permute-start | bytes 393224 | tf_op jit(solution)/shard_map/ppermute | solution.py:37
  68.4 9.9 %collective-permute-start.35 = (bf16[8,64,128]{2,1,0:T(8,128)(2,1)S(1)}, bf16[8,64,128]{2,1,0:T(8,128)(2,1)S(1)}, u32[]{:S(2)}, u32[]{:S(2)}) collective-permute-start(bf16[8,64,128]{2,1,0:T(8,128)(2,1)S(1)} %get-tuple-element.69.refs_0_.refs_4_), channel_id=1, source_target_pairs={{0,16},{8,24},{16,0},{24,8},{1,17},{9,25},{17,1},{25,9},{2,18},{10... | collective-permute-start | bytes 393224 | tf_op jit(solution)/shard_map/ppermute | solution.py:37
  72.3 6.0 %collective-permute-start.34 = (bf16[7,64,128]{2,1,0:T(8,128)(2,1)S(1)}, bf16[7,64,128]{2,1,0:T(8,128)(2,1)S(1)}, u32[]{:S(2)}, u32[]{:S(2)}) collective-permute-start(bf16[7,64,128]{2,1,0:T(8,128)(2,1)S(1)} %slice.22), channel_id=1, source_target_pairs={{0,8},{8,0},{16,24},{24,16},{1,9},{9,1},{17,25},{25,17},{2,10},{10... | collective-permute-start | bytes 344072 | tf_op jit(solution)/shard_map/ppermute | solution.py:37
  72.4 7.2 %collective-permute-start.39 = (bf16[8,64,128]{2,1,0:T(8,128)(2,1)S(1)}, bf16[8,64,128]{2,1,0:T(8,128)(2,1)S(1)}, u32[]{:S(2)}, u32[]{:S(2)}) collective-permute-start(bf16[8,64,128]{2,1,0:T(8,128)(2,1)S(1)} %get-tuple-element.69.refs_0_.refs_4_), channel_id=1, source_target_pairs={{0,6},{1,7},{2,4},{3,5},{4,2},{5,3},{6,0},{7,1},{8,14},{9,15},{10,... | collective-permute-start | bytes 393224 | tf_op jit(solution)/shard_map/ppermute | solution.py:37
  74.9 5.7 %collective-permute-start.38 = (bf16[8,64,128]{2,1,0:T(8,128)(2,1)S(1)}, bf16[8,64,128]{2,1,0:T(8,128)(2,1)S(1)}, u32[]{:S(2)}, u32[]{:S(2)}) collective-permute-start(bf16[8,64,128]{2,1,0:T(8,128)(2,1)S(1)} %get-tuple-element.69.refs_0_.refs_4_), channel_id=1, source_target_pairs={{0,4},{1,5},{2,6},{3,7},{4,0},{5,1},{6,2},{7,3},{8,12},{9,13},{10,... | collective-permute-start | bytes 393224 | tf_op jit(solution)/shard_map/ppermute | solution.py:37
  75.4 5.3 %collective-permute-start.37 = (bf16[8,64,128]{2,1,0:T(8,128)(2,1)S(1)}, bf16[8,64,128]{2,1,0:T(8,128)(2,1)S(1)}, u32[]{:S(2)}, u32[]{:S(2)}) collective-permute-start(bf16[8,64,128]{2,1,0:T(8,128)(2,1)S(1)} %get-tuple-element.69.refs_0_.refs_4_), channel_id=1, source_target_pairs={{0,2},{1,3},{2,0},{3,1},{4,6},{5,7},{6,4},{7,5},{8,10},{9,11},{10,... | collective-permute-start | bytes 393224 | tf_op jit(solution)/shard_map/ppermute | solution.py:37
  78.3 5.2 %collective-permute-start.36 = (bf16[9,64,128]{2,1,0:T(8,128)(2,1)S(1)}, bf16[9,64,128]{2,1,0:T(8,128)(2,1)S(1)}, u32[]{:S(2)}, u32[]{:S(2)}) collective-permute-start(bf16[9,64,128]{2,1,0:T(8,128)(2,1)S(1)} %pad_maximum_fusion.2), channel_id=1, source_target_pairs={{0,8},{8,0},{16,24},{24,16},{1,9},{9,1},{17,25},{25,17},{2,10},{10... | collective-permute-start | bytes 442376 | tf_op jit(solution)/shard_map/ppermute | solution.py:37
  79.6 1.5 %collective-permute-start.40 = (bf16[8,64,128]{2,1,0:T(8,128)(2,1)S(1)}, bf16[8,64,128]{2,1,0:T(8,128)(2,1)S(1)}, u32[]{:S(2)}, u32[]{:S(2)}) collective-permute-start(bf16[8,64,128]{2,1,0:T(8,128)(2,1)S(1)} %get-tuple-element.69.refs_0_.refs_4_), channel_id=1, source_target_pairs={{0,1},{1,0},{2,3},{3,2},{4,5},{5,4},{6,7},{7,6},{8,9},{9,8},{10,11... | collective-permute-start | bytes 393224 | tf_op jit(solution)/shard_map/ppermute | solution.py:37
  79.6 1.5 %collective-permute-start.43 = (bf16[8,64,128]{2,1,0:T(8,128)(2,1)S(1)}, bf16[8,64,128]{2,1,0:T(8,128)(2,1)S(1)}, u32[]{:S(2)}, u32[]{:S(2)}) collective-permute-start(bf16[8,64,128]{2,1,0:T(8,128)(2,1)S(1)} %collective-permute-done.39.refs_7_), channel_id=1, source_target_pairs={{0,1},{1,0},{2,3},{3,2},{4,5},{5,4},{6,7},{7,6},{8,9},{9,8},{10,11... | collective-permute-start | bytes 393224 | tf_op jit(solution)/shard_map/ppermute | solution.py:37
  80.7 1.4 %collective-permute-start.41 = (bf16[8,64,128]{2,1,0:T(8,128)(2,1)S(1)}, bf16[8,64,128]{2,1,0:T(8,128)(2,1)S(1)}, u32[]{:S(2)}, u32[]{:S(2)}) collective-permute-start(bf16[8,64,128]{2,1,0:T(8,128)(2,1)S(1)} %collective-permute-done.37.refs_5_), channel_id=1, source_target_pairs={{0,1},{1,0},{2,3},{3,2},{4,5},{5,4},{6,7},{7,6},{8,9},{9,8},{10,11... | collective-permute-start | bytes 393224 | tf_op jit(solution)/shard_map/ppermute | solution.py:37
  86.8 4.7 %collective-permute-start.47 = (f32[40,128]{1,0:T(8,128)S(1)}, f32[40,128]{1,0:T(8,128)S(1)}, u32[]{:S(2)}, u32[]{:S(2)}) collective-permute-start(f32[40,128]{1,0:T(8,128)S(1)} %add.76), channel_id=1, source_target_pairs={{0,6},{1,7},{2,4},{3,5},{4,2},{5,3},{6,0},{7,1},{8,14},{9,15},{10,... | collective-permute-start | bytes 61448 | tf_op jit(solution)/shard_map/ppermute | solution.py:37
  89.2 3.8 %collective-permute-start.46 = (f32[40,128]{1,0:T(8,128)S(1)}, f32[40,128]{1,0:T(8,128)S(1)}, u32[]{:S(2)}, u32[]{:S(2)}) collective-permute-start(f32[40,128]{1,0:T(8,128)S(1)} %add.76), channel_id=1, source_target_pairs={{0,4},{1,5},{2,6},{3,7},{4,0},{5,1},{6,2},{7,3},{8,12},{9,13},{10,... | collective-permute-start | bytes 61448 | tf_op jit(solution)/shard_map/ppermute | solution.py:37
  89.8 3.8 %collective-permute-start.45 = (f32[40,128]{1,0:T(8,128)S(1)}, f32[40,128]{1,0:T(8,128)S(1)}, u32[]{:S(2)}, u32[]{:S(2)}) collective-permute-start(f32[40,128]{1,0:T(8,128)S(1)} %add.76), channel_id=1, source_target_pairs={{0,2},{1,3},{2,0},{3,1},{4,6},{5,7},{6,4},{7,5},{8,10},{9,11},{10,... | collective-permute-start | bytes 61448 | tf_op jit(solution)/shard_map/ppermute | solution.py:37
  93.5 5.7 %collective-permute-start.50 = (f32[40,128]{1,0:T(8,128)S(1)}, f32[40,128]{1,0:T(8,128)S(1)}, u32[]{:S(2)}, u32[]{:S(2)}) collective-permute-start(f32[40,128]{1,0:T(8,128)S(1)} %add_add_fusion.refs_0_), channel_id=1, source_target_pairs={{0,24},{8,16},{16,8},{24,0},{1,25},{9,17},{17,9},{25,1},{2,26},{10... | collective-permute-start | bytes 61448 | tf_op jit(solution)/shard_map/ppermute | solution.py:37
  94.5 5.1 %collective-permute-start.49 = (f32[40,128]{1,0:T(8,128)S(1)}, f32[40,128]{1,0:T(8,128)S(1)}, u32[]{:S(2)}, u32[]{:S(2)}) collective-permute-start(f32[40,128]{1,0:T(8,128)S(1)} %add_add_fusion.refs_0_), channel_id=1, source_target_pairs={{0,16},{8,24},{16,0},{24,8},{1,17},{9,25},{17,1},{25,9},{2,18},{10... | collective-permute-start | bytes 61448 | tf_op jit(solution)/shard_map/ppermute | solution.py:37
  96.2 3.8 %collective-permute-start.48 = (f32[40,128]{1,0:T(8,128)S(1)}, f32[40,128]{1,0:T(8,128)S(1)}, u32[]{:S(2)}, u32[]{:S(2)}) collective-permute-start(f32[40,128]{1,0:T(8,128)S(1)} %add_add_fusion.refs_0_), channel_id=1, source_target_pairs={{0,8},{8,0},{16,24},{24,16},{1,9},{9,1},{17,25},{25,17},{2,10},{10... | collective-permute-start | bytes 61448 | tf_op jit(solution)/shard_map/ppermute | solution.py:37
  (9 other events, 25.1 us)

commit v10 on v9

--- a/solution.py
+++ b/solution.py
@@ -16,20 +16,21 @@
 F32 = jnp.float32
 VMEM = pl.BlockSpec(memory_space=pltpu.VMEM)
 SMEM = pl.BlockSpec(memory_space=pltpu.SMEM)
+ANY = pl.BlockSpec(memory_space=pl.ANY)
 DEGREE_ROWS = 16
 
 
-def call(kernel, out_shape, scratch, limit, args, flops=0, smem=0):
+def call(kernel, out_shape, scratch, limit, args, flops=0, smem=0, after=()):
     moved = sum(x.size * x.dtype.itemsize for x in args)
     return pl.pallas_call(
-        kernel,
+        lambda *refs: kernel(*refs[len(after) :]),
         out_shape=out_shape,
-        in_specs=[SMEM] * smem + [VMEM] * (len(args) - smem),
+        in_specs=[ANY] * len(after) + [SMEM] * smem + [VMEM] * (len(args) - smem),
         out_specs=jax.tree.map(lambda _: VMEM, out_shape),
         scratch_shapes=scratch,
         compiler_params=pltpu.CompilerParams(vmem_limit_bytes=limit * 2**20),
         cost_estimate=pl.CostEstimate(flops=flops, bytes_accessed=moved, transcendentals=0),
-    )(*args)
+    )(*after, *args)
 
 
 def trade(part, axis, d):
@@ -46,9 +47,18 @@
     return [ref[:, k * width : (k + 1) * width] for k in range(ref.shape[1] // width)]
 
 
-def round_kernel(vec_ref, out_ref):
-    for k, piece in enumerate(tiles_first(vec_ref, out_ref.shape[2])):
+def round_kernel(meta, rows_ref, cols_ref, vec_ref, out_ref, table_ref):
+    group, _, width = out_ref.shape
+    for k, piece in enumerate(tiles_first(vec_ref, width)):
         out_ref[k] = piece.astype(BF16)
+    rows, cols = rows_ref[...], cols_ref[...]
+    col_apart = lax.div(cols, group) ^ meta[0]
+    row_apart = lax.div(rows, group) ^ meta[1]
+    row_halves = lax.rem(row_apart, 2) * meta[2] + lax.div(row_apart, 2)
+    inside = lax.rem(rows, group)
+    table_ref[0:1, :] = col_apart * group + lax.rem(cols, group)
+    table_ref[1:2, :] = row_apart * group + inside
+    table_ref[2:3, :] = row_halves * group + inside
 
 
 def split_degree(sums):
@@ -79,63 +89,89 @@
             ref[pl.ds(place, 1), :] += sums[:1]
 
 
-def product_kernel(runs, order, degree, table, tiles_ref, *refs):
-    col_runs, row_runs = runs
-    half = len(row_runs) // 2
-    col_parts, refs = refs[: len(col_runs)], refs[len(col_runs) :]
-    row_parts, refs = refs[: len(row_runs)], refs[len(row_runs) :]
+def column_kernel(runs, degree, table, tiles_ref, *refs):
+    parts, refs = refs[: len(runs)], refs[len(runs) :]
     if degree:
-        row_degree, col_degree, *refs = refs
-    kept_ref, swap_ref, own_ref, *send_refs = refs[:-4]
-    col_panel, row_panel, row_total, col_total = refs[-4:]
-    group, vectors_n, width = col_parts[0].shape
-    fill(col_panel, col_parts, col_runs)
-    fill(row_panel, row_parts, row_runs)
-    row_total[...] = jnp.zeros_like(row_total)
-    col_total[...] = jnp.zeros_like(col_total)
+        sums, *refs = refs
+    own_ref, *send_refs, panel, total = refs
+    group, vectors_n, _ = own_ref.shape
+    fill(panel, parts, runs)
+    total[...] = jnp.zeros_like(total)
     for t in range(tiles_ref.shape[0]):
-        tile, here = tiles_ref[t], table[0, t]
-        row_total[table[2, t]] += lax.dot_general(
-            col_panel[here], tile, NT, preferred_element_type=F32
+        total[table[0, t]] += lax.dot_general(
+            panel[table[1, t]], tiles_ref[t], NN, preferred_element_type=F32
         )
-        col_total[here] += lax.dot_general(
-            row_panel[table[1, t]], tile, NN, preferred_element_type=F32
+    own_ref[...] = total[:group]
+    for d, send in enumerate(send_refs, 1):
+        round_sums(send, total, d * group, group)
+        if degree:
+            send[group * vectors_n :, :] = split_degree(sums[d * group : (d + 1) * group, :])
+
+
+def row_kernel(runs, degree, table, tiles_ref, *refs):
+    parts, refs = refs[: len(runs)], refs[len(runs) :]
+    if degree:
+        sums, *refs = refs
+    kept_ref, swap_ref, panel, total = refs
+    half, group, vectors_n, _ = kept_ref.shape
+    fill(panel, parts, runs)
+    total[...] = jnp.zeros_like(total)
+    for t in range(tiles_ref.shape[0]):
+        total[table[2, t]] += lax.dot_general(
+            panel[table[0, t]], tiles_ref[t], NT, preferred_element_type=F32
         )
     for d in range(half):
-        kept_ref[d] = row_total[d * group : (d + 1) * group]
-    own_ref[...] = col_total[:group]
-    sends = [(row_total, half + d, swap_ref.at[d]) for d in range(half)]
-    sends += [(col_total, d, send) for d, send in zip(order, send_refs)]
-    for total, d, send in sends:
-        for k in range(group):
-            send[k * vectors_n : (k + 1) * vectors_n, :] = total[d * group + k].astype(BF16)
+        kept_ref[d] = total[d * group : (d + 1) * group]
+        round_sums(swap_ref.at[d], total, (half + d) * group, group)
         if degree:
-            sums = row_degree if total is row_total else col_degree
-            send[group * vectors_n :, :] = split_degree(sums[d * group : (d + 1) * group, :])
-
-
-def products(tiles, table, col_parts, row_parts, runs, order, degree):
+            rows = slice((half + d) * group, (half + d + 1) * group)
+            swap_ref[d, group * vectors_n :, :] = split_degree(sums[rows, :])
+
+
+def round_sums(send, total, start, group):
+    vectors_n = total.shape[1]
+    for k in range(group):
+        send[k * vectors_n : (k + 1) * vectors_n, :] = total[start + k].astype(BF16)
+
+
+def products(tiles, table, col_parts, row_parts, runs, degree):
     group, vectors_n, width = col_parts[0].shape
-    rows_n, half = len(order) + 1, len(row_parts) // 2
+    half = len(row_parts) // 2
+    rows_n = max(place + count for run in runs[0] for place, count in run) // group
     rows = group * vectors_n + (2 * group if degree else 0)
-    out_shape = [
-        jax.ShapeDtypeStruct((half, group, vectors_n, width), F32),
-        jax.ShapeDtypeStruct((half, rows, width), BF16),
-        jax.ShapeDtypeStruct((group, vectors_n, width), F32),
-    ]
-    out_shape += [jax.ShapeDtypeStruct((rows, width), BF16)] * (rows_n - 1)
-    scratch = [
-        pltpu.VMEM((rows_n * group, vectors_n, width), BF16),
-        pltpu.VMEM((2 * half * group, vectors_n, width), BF16),
-        pltpu.VMEM((2 * half * group, vectors_n, width), F32),
-        pltpu.VMEM((rows_n * group, vectors_n, width), F32),
-    ]
-    kernel = functools.partial(product_kernel, runs, order, bool(degree))
-    args = [table, tiles, *col_parts, *row_parts, *degree]
-    kept, swap, own, *send = call(
-        kernel, out_shape, scratch, 32, args, 4 * tiles.size * vectors_n, 1
-    )
-    return kept, swap, own, send
+    own_shape = jax.ShapeDtypeStruct((group, vectors_n, width), F32)
+    send_shape = jax.ShapeDtypeStruct((rows, width), BF16)
+    flops = 2 * tiles.size * vectors_n
+
+    def panels(source, target):
+        return [
+            pltpu.VMEM((source * group, vectors_n, width), BF16),
+            pltpu.VMEM((target * group, vectors_n, width), F32),
+        ]
+
+    col_own, *col_send = call(
+        functools.partial(column_kernel, runs[1], bool(degree)),
+        [own_shape] + [send_shape] * (rows_n - 1),
+        panels(2 * half, rows_n),
+        24,
+        [table, tiles, *row_parts, *degree[1:]],
+        flops,
+        1,
+    )
+    kept, swap = call(
+        functools.partial(row_kernel, runs[0], bool(degree)),
+        [
+            jax.ShapeDtypeStruct((half, group, vectors_n, width), F32),
+            jax.ShapeDtypeStruct((half, rows, width), BF16),
+        ],
+        panels(rows_n, 2 * half),
+        24,
+        [table, tiles, *col_parts, *degree[:1]],
+        flops,
+        1,
+        [col_own],
+    )
+    return kept, swap, col_own, col_send
 
 
 def merge_kernel(degree, kept, got, *refs):
@@ -215,19 +251,22 @@
     )
 
 
-def form_kernel(runs, table, tiles_ref, gram_ref, *refs):
-    col_end = len(runs[0])
-    col_parts, row_parts = refs[:col_end], refs[col_end:-5]
-    out_ref, col_panel, row_panel, left, right = refs[-5:]
-    _, vectors_n, width = col_panel.shape
-    fill(col_panel, col_parts, runs[0])
-    fill(row_panel, row_parts, runs[1])
+def half_form_kernel(runs, table, tiles_ref, *refs):
+    parts, (out_ref, panel) = refs[:-2], refs[-2:]
+    width = panel.shape[2]
+    fill(panel, parts, runs)
     for t in range(tiles_ref.shape[0]):
-        columns = slice(t * width, (t + 1) * width)
-        left[:, columns] = row_panel[table[1, t]]
-        right[:, columns] = lax.dot_general(
-            col_panel[table[0, t]], tiles_ref[t], NT, preferred_element_type=F32
+        out_ref[:, t * width : (t + 1) * width] = lax.dot_general(
+            panel[table[1, t]], tiles_ref[t], NN, preferred_element_type=F32
         ).astype(BF16)
+
+
+def form_kernel(runs, table, left, gram_ref, *refs):
+    parts, (out_ref, panel, right) = refs[:-3], refs[-3:]
+    _, vectors_n, width = panel.shape
+    fill(panel, parts, runs)
+    for t in range(right.shape[1] // width):
+        right[:, t * width : (t + 1) * width] = panel[table[0, t]]
     form = lax.dot_general(left[...], right[...], NT, preferred_element_type=F32)
     projected = gram_ref[:, vectors_n:] - 0.5 * (form + form.T)
     row, col = square_index(vectors_n)
@@ -251,10 +290,11 @@
     below = lax.broadcasted_iota(jnp.int32, (8, 2 * n), 0)
     for j in range(n):
         at, line = j // 8, j % 8
-        pivot_row = bands[at][line : line + 1, :]
-        pivot_row = jnp.broadcast_to(pivot_row / pivot_row[:, j : j + 1], (8, 2 * n))
+        lanes = {i: jnp.broadcast_to(bands[i][:, j : j + 1], below.shape) for i in range(at, n // 8)}
+        pivot_row = bands[at][line : line + 1, :] * (1.0 / lanes[at][line : line + 1, :])
+        pivot_row = jnp.broadcast_to(pivot_row, below.shape)
         for i in range(at, n // 8):
-            update = bands[i][:, j : j + 1] * pivot_row
+            update = lanes[i] * pivot_row
             if i == at:
                 update = jnp.where(below > line, update, 0.0)
             bands[i] = bands[i] - update
@@ -283,7 +323,7 @@
     half_way = dot(inverse, projected, NN)
     rayleigh_ref[...] = dot(half_way, inverse, NT)
     turned = dot(inverse, half_way, NT)
-    ritz_ref[...] = dot(dot(turned, inverse, NN), filtered_ref[...], NN)
+    ritz_ref[...] = dot(turned, dot(inverse, filtered_ref[...], NN), NN)
 
 
 def tree_sum(parts):
@@ -305,12 +345,6 @@
     rounded_shape = jax.ShapeDtypeStruct((group, vectors_n, width), BF16)
     vector_shape = jax.ShapeDtypeStruct((vectors_n, own_nodes), F32)
     degree_shape = jax.ShapeDtypeStruct((group, width), F32)
-
-    col_apart = (tile_cols // group) ^ lax.axis_index("row")
-    row_apart = (tile_rows // group) ^ lax.axis_index("col")
-    row_halves = row_apart % 2 * chips_n + row_apart // 2
-    table = jnp.stack([col_apart, row_apart, row_halves]) * group
-    table = (table + jnp.stack([tile_cols, tile_rows, tile_rows]) % group).astype(jnp.int32)
 
     late = 1
     levels = [rows_n >> i for i in range(1, rows_n.bit_length())]
@@ -324,8 +358,6 @@
         col_runs += [[(d * group, cut)], [(d * group + cut, late), *passed]]
     row_runs = [[((2 * d + core) * group, group)] for core in range(2) for d in range(chips_n)]
     runs = (col_runs, row_runs)
-    order = [*range(1, rows_n)]
-
     def gather(rounded, first=()):
         held = [rounded]
         for d in levels:
@@ -340,10 +372,8 @@
         return held, chips + [trade(chip, "col", 1) for chip in chips]
 
     def apply(rounded, degree=()):
-        kept, swap, col_own, col_send = products(
-            tiles, table, *gather(rounded), runs, order, degree
-        )
-        col_got = [trade(part, "row", d) for d, part in zip(order, col_send)]
+        kept, swap, col_own, col_send = products(tiles, table, *gather(rounded), runs, degree)
+        col_got = exchange(col_send, "row")
         row_own, *row_send = merge(kept, trade(swap, "col", 1), degree)
         if degree:
             own_degree, *row_send = row_send
@@ -351,7 +381,15 @@
         sums = [row_own, col_own, *row_got, *col_got]
         return [own_degree, degree[1], *sums] if degree else sums
 
-    rounded = call(round_kernel, rounded_shape, [], 16, [start])
+    meta = jnp.stack([lax.axis_index("row"), lax.axis_index("col"), chips_n]).astype(jnp.int32)
+    rounded, table = call(
+        round_kernel,
+        [rounded_shape, jax.ShapeDtypeStruct((3, tiles.shape[0]), jnp.int32)],
+        [],
+        16,
+        [meta, tile_rows[None], tile_cols[None], start],
+        smem=1,
+    )
     degree = call(
         degree_kernel,
         [jax.ShapeDtypeStruct((n * group, width), F32) for n in (cols_n, rows_n)],
@@ -376,18 +414,22 @@
         [start, first, degree, *apply(rounded)],
     )
     col_parts, row_parts = gather(rounded)
+    left = call(
+        functools.partial(half_form_kernel, runs[1]),
+        jax.ShapeDtypeStruct(spread, BF16),
+        [pltpu.VMEM((cols_n * group, vectors_n, width), BF16)],
+        24,
+        [table, tiles, *row_parts],
+        2 * tiles.size * vectors_n,
+        1,
+    )
     sums = call(
-        functools.partial(form_kernel, runs),
+        functools.partial(form_kernel, runs[0]),
         jax.ShapeDtypeStruct((vectors_n // 2 + 8, 2 * vectors_n), F32),
-        [
-            pltpu.VMEM((rows_n * group, vectors_n, width), BF16),
-            pltpu.VMEM((cols_n * group, vectors_n, width), BF16),
-            pltpu.VMEM(spread, BF16),
-            pltpu.VMEM(spread, BF16),
-        ],
-        24,
-        [table, tiles, gram, *col_parts, *row_parts],
-        4 * tiles.size * vectors_n,
+        [pltpu.VMEM((rows_n * group, vectors_n, width), BF16), pltpu.VMEM(spread, BF16)],
+        24,
+        [table, left, gram, *col_parts],
+        2 * vectors_n * spread[0] * spread[1],
         1,
     )
     sums = sums + trade(sums, "col", 1)

time: 107 us -> 106 us (level)
  starting transfers between devices: 57.7 us -> 54.7 us
  Pallas kernels: 15.7 us -> 17.9 us
    ppermute x51, starting transfers between devices: 57.7 us -> 54.7 us  [trade(): return lax.ppermute(part, axis, [(i, i ^ d) for i in range(n)])]
    pallas_call x10 -> x13, Pallas kernels: 15.7 us -> 17.9 us  [call(): pl.pallas_call(lambda *refs: kernel(*refs[len(after):]), out_shape=out_sh...]
  transfers between devices with their start and end apart: 51 -> 51, of which waited for: 24 -> 30; matrix products, arithmetic and copies ran while one was open for 0% -> 0% of each run, Pallas kernels for 2% -> 5%
where the time goes in v10:
time: 106 us; the launch traced here: 105 us
  starting transfers between devices  54.7 us (52%)
  waiting for transfers between devices  29 us (27%)
  Pallas kernels  17.9 us (17%)
  local copies, waits for them, and re-layouts  2.88 us (3%)
    ppermute x51, starting transfers between devices, trade(): return lax.ppermute(part, axis, [(i, i ^ d) for i in range(n)])  54.7 us
    ppermute x51, waiting for transfers between devices, trade(): return lax.ppermute(part, axis, [(i, i ^ d) for i in range(n)])  29 us
    pallas_call x13, Pallas kernels, call(): pl.pallas_call(lambda *refs: kernel(*refs[len(after):]), out_shape=out_sh...  17.9 us
    unnamed x12, local copies, waits for them, and re-layouts  2.85 us
  transfers between devices with their start and end apart: 51, of which 30 were waited for; matrix products, arithmetic and copies ran while one was open for 0% of the time, Pallas kernels for 5%

profile of v10, /device:TPU:0, one launch (start us, length us, event | category | flops | bytes accessed | tf_op | source)
XLA Modules:
  0.0 105.4 jit_solution(188928263615908701)
XLA Ops:
  1.4 0.9 copy-done.2
  2.9 4.1 %collective-permute-start.8 = (bf16[8,64,128]{2,1,0:T(8,128)(2,1)S(1)}, bf16[8,64,128]{2,1,0:T(8,128)(2,1)S(1)}, u32[]{:S(2)}, u32[]{:S(2)}) collective-permute-start(bf16[8,64,128]{2,1,0:T(8,128)(2,1)S(1)} %get-tuple-element.40.refs_2_.refs_3_), channel_id=1, source_target_pairs={{0,16},{8,24},{16,0},{24,8},{1,17},{9,25},{17,1},{25,9},{2,18},{10... | collective-permute-start | bytes 393224 | tf_op jit(solution)/shard_map/ppermute | solution.py:38
  7.0 1.6 %collective-permute-start.7 = (bf16[7,64,128]{2,1,0:T(8,128)(2,1)S(1)}, bf16[7,64,128]{2,1,0:T(8,128)(2,1)S(1)}, u32[]{:S(2)}, u32[]{:S(2)}) collective-permute-start(bf16[7,64,128]{2,1,0:T(8,128)(2,1)S(1)} %slice.18), channel_id=1, source_target_pairs={{0,8},{8,0},{16,24},{24,16},{1,9},{9,1},{17,25},{25,17},{2,10},{10... | collective-permute-start | bytes 344072 | tf_op jit(solution)/shard_map/ppermute | solution.py:38
  8.7 2.4 %collective-permute-start.2 = (bf16[8,64,128]{2,1,0:T(8,128)(2,1)S(1)}, bf16[8,64,128]{2,1,0:T(8,128)(2,1)S(1)}, u32[]{:S(2)}, u32[]{:S(2)}) collective-permute-start(bf16[8,64,128]{2,1,0:T(8,128)(2,1)S(1)} %get-tuple-element.40.refs_2_.refs_3_), channel_id=1, source_target_pairs={{0,6},{1,7},{2,4},{3,5},{4,2},{5,3},{6,0},{7,1},{8,14},{9,15},{10,... | collective-permute-start | bytes 393224 | tf_op jit(solution)/shard_map/ppermute | solution.py:38
  12.2 1.4 %collective-permute-done.7.refs_5_ = bf16[7,64,128]{2,1,0:T(8,128)(2,1)S(1)} collective-permute-done((bf16[7,64,128]{2,1,0:T(8,128)(2,1)S(1)}, bf16[7,64,128]{2,1,0:T(8,128)(2,1)S(1)}, u32[]{:S(2)}, u32[]{:S(2)}) %collective-permute-start.7) | collective-permute-done | bytes 114720 | tf_op jit(solution)/shard_map/ppermute | solution.py:38
  13.5 1.3 %collective-permute-start.9 = (bf16[9,64,128]{2,1,0:T(8,128)(2,1)S(1)}, bf16[9,64,128]{2,1,0:T(8,128)(2,1)S(1)}, u32[]{:S(2)}, u32[]{:S(2)}) collective-permute-start(bf16[9,64,128]{2,1,0:T(8,128)(2,1)S(1)} %pad_maximum_fusion), channel_id=1, source_target_pairs={{0,8},{8,0},{16,24},{24,16},{1,9},{9,1},{17,25},{25,17},{2,10},{10... | collective-permute-start | bytes 442376 | tf_op jit(solution)/shard_map/ppermute | solution.py:38
  15.3 1.7 %collective-permute-done.1.refs_4_ = bf16[8,64,128]{2,1,0:T(8,128)(2,1)S(1)} collective-permute-done((bf16[8,64,128]{2,1,0:T(8,128)(2,1)S(1)}, bf16[8,64,128]{2,1,0:T(8,128)(2,1)S(1)}, u32[]{:S(2)}, u32[]{:S(2)}) %collective-permute-start.1) | collective-permute-done | bytes 131104 | tf_op jit(solution)/shard_map/ppermute | solution.py:38
  17.6 1.2 %copy-done = bf16[1,1,32,128,128]{4,3,2,1,0:T(8,128)(2,1)S(1)} copy-done((bf16[1,1,32,128,128]{4,3,2,1,0:T(8,128)(2,1)S(1)}, bf16[1,1,32,128,128]{4,3,2,1,0:T(8,128)(2,1)}, u32[]{:S(2)}) %copy-start) | copy-done | bytes 1048600
  18.8 1.5 %shard_map.60 = (f32[64,128]{1,0:T(8,128)S(1)}, f32[32,128]{1,0:T(8,128)S(1)}) custom-call(s32[3,32]{1,0:T(4,128)S(1)} %get-tuple-element.39.refs_0_.refs_1_, bf16[32,128,128]{2,1,0:T(8,128)(2,1)S(1)} %bitcast.5), custom_call_target="tpu_custom_call" | custom-call | flops 33554432 | bytes 1048960 | tf_op jit(solution)/shard_map/pallas_call | solution.py:25
  20.4 1.1 %shard_map.61 = (f32[8,64,128]{2,1,0:T(8,128)S(1)}, bf16[528,128]{1,0:T(8,128)(2,1)S(1)}, bf16[528,128]{1,0:T(8,128)(2,1)S(1)}, bf16[528,128]{1,0:T(8,128)(2,1)S(1)}) custom-call(s32[3,32]{1,0:T(4,128)S(1)} %get-tuple-element.39.refs_0_.refs_1_, bf16[32,128,128]{2,1,0:T(8,128)(2,1)S(1)} %bitcast.6, ...), custom_call_target="tpu_custom_call" | custom-call | flops 67108864 | bytes 2113920 | tf_op jit(solution)/shard_map/pallas_call | solution.py:25
  21.5 1.5 %shard_map.62 = (f32[4,8,64,128]{3,2,1,0:T(8,128)S(1)}, bf16[4,528,128]{2,1,0:T(8,128)(2,1)S(1)}) custom-call(f32[8,64,128]{2,1,0:T(8,128)S(1)} %get-tuple-element.42.refs_0_.refs_4_, s32[3,32]{1,0:T(4,128)S(1)} %get-tuple-element.39.refs_0_.refs_1_, bf16[32,128,128]{2,1,0:T(8,128)(2,1)S(1)} %bitcast.7, ...), custom_call_target="tpu_custom_call" | custom-call | flops 67108864 | bytes 1606016 | tf_op jit(solution)/shard_map/pallas_call | solution.py:25
  23.6 1.3 %collective-permute-start.15 = (bf16[528,128]{1,0:T(8,128)(2,1)S(1)}, bf16[528,128]{1,0:T(8,128)(2,1)S(1)}, u32[]{:S(2)}, u32[]{:S(2)}) collective-permute-start(bf16[528,128]{1,0:T(8,128)(2,1)S(1)} %get-tuple-element.54), channel_id=1, source_target_pairs={{0,16},{8,24},{16,0},{24,8},{1,17},{9,25},{17,1},{25,9},{2,18},{10... | collective-permute-start | bytes 405512 | tf_op jit(solution)/shard_map/ppermute | solution.py:38
  24.9 2.6 %collective-permute-start.16 = (bf16[528,128]{1,0:T(8,128)(2,1)S(1)}, bf16[528,128]{1,0:T(8,128)(2,1)S(1)}, u32[]{:S(2)}, u32[]{:S(2)}) collective-permute-start(bf16[528,128]{1,0:T(8,128)(2,1)S(1)} %get-tuple-element.55), channel_id=1, source_target_pairs={{0,24},{8,16},{16,8},{24,0},{1,25},{9,17},{17,9},{25,1},{2,26},{10... | collective-permute-start | bytes 405512 | tf_op jit(solution)/shard_map/ppermute | solution.py:38
  27.7 1.6 %collective-permute-start.11 = (bf16[528,128]{1,0:T(8,128)(2,1)S(1)}, bf16[528,128]{1,0:T(8,128)(2,1)S(1)}, u32[]{:S(2)}, u32[]{:S(2)}) collective-permute-start(bf16[528,128]{1,0:T(8,128)(2,1)S(1)} %get-tuple-element.50), channel_id=1, source_target_pairs={{0,2},{1,3},{2,0},{3,1},{4,6},{5,7},{6,4},{7,5},{8,10},{9,11},{10,... | collective-permute-start | bytes 405512 | tf_op jit(solution)/shard_map/ppermute | solution.py:38
  30.1 1.2 %collective-permute-done.14.refs_8_ = bf16[528,128]{1,0:T(8,128)(2,1)S(1)} collective-permute-done((bf16[528,128]{1,0:T(8,128)(2,1)S(1)}, bf16[528,128]{1,0:T(8,128)(2,1)S(1)}, u32[]{:S(2)}, u32[]{:S(2)}) %collective-permute-start.14) | collective-permute-done | bytes 135200 | tf_op jit(solution)/shard_map/ppermute | solution.py:38
  31.3 2.1 %collective-permute-start.13 = (bf16[528,128]{1,0:T(8,128)(2,1)S(1)}, bf16[528,128]{1,0:T(8,128)(2,1)S(1)}, u32[]{:S(2)}, u32[]{:S(2)}) collective-permute-start(bf16[528,128]{1,0:T(8,128)(2,1)S(1)} %get-tuple-element.52), channel_id=1, source_target_pairs={{0,6},{1,7},{2,4},{3,5},{4,2},{5,3},{6,0},{7,1},{8,14},{9,15},{10,... | collective-permute-start | bytes 405512 | tf_op jit(solution)/shard_map/ppermute | solution.py:38
  33.4 3.4 %collective-permute-done.15.refs_9_ = bf16[528,128]{1,0:T(8,128)(2,1)S(1)} collective-permute-done((bf16[528,128]{1,0:T(8,128)(2,1)S(1)}, bf16[528,128]{1,0:T(8,128)(2,1)S(1)}, u32[]{:S(2)}, u32[]{:S(2)}) %collective-permute-start.15) | collective-permute-done | bytes 135200 | tf_op jit(solution)/shard_map/ppermute | solution.py:38
  37.5 2.7 %collective-permute-start.25 = (bf16[8,64,128]{2,1,0:T(8,128)(2,1)S(1)}, bf16[8,64,128]{2,1,0:T(8,128)(2,1)S(1)}, u32[]{:S(2)}, u32[]{:S(2)}) collective-permute-start(bf16[8,64,128]{2,1,0:T(8,128)(2,1)S(1)} %get-tuple-element.58.refs_2_.refs_3_), channel_id=1, source_target_pairs={{0,16},{8,24},{16,0},{24,8},{1,17},{9,25},{17,1},{25,9},{2,18},{10... | collective-permute-start | bytes 393224 | tf_op jit(solution)/shard_map/ppermute | solution.py:38
  40.4 2.5 %collective-permute-start.19 = (bf16[8,64,128]{2,1,0:T(8,128)(2,1)S(1)}, bf16[8,64,128]{2,1,0:T(8,128)(2,1)S(1)}, u32[]{:S(2)}, u32[]{:S(2)}) collective-permute-start(bf16[8,64,128]{2,1,0:T(8,128)(2,1)S(1)} %get-tuple-element.58.refs_2_.refs_3_), channel_id=1, source_target_pairs={{0,6},{1,7},{2,4},{3,5},{4,2},{5,3},{6,0},{7,1},{8,14},{9,15},{10,... | collective-permute-start | bytes 393224 | tf_op jit(solution)/shard_map/ppermute | solution.py:38
  43.9 2.1 %collective-permute-done.24.refs_5_ = bf16[7,64,128]{2,1,0:T(8,128)(2,1)S(1)} collective-permute-done((bf16[7,64,128]{2,1,0:T(8,128)(2,1)S(1)}, bf16[7,64,128]{2,1,0:T(8,128)(2,1)S(1)}, u32[]{:S(2)}, u32[]{:S(2)}) %collective-permute-start.24) | collective-permute-done | bytes 114720 | tf_op jit(solution)/shard_map/ppermute | solution.py:38
  46.3 1.4 %collective-permute-start.26 = (bf16[9,64,128]{2,1,0:T(8,128)(2,1)S(1)}, bf16[9,64,128]{2,1,0:T(8,128)(2,1)S(1)}, u32[]{:S(2)}, u32[]{:S(2)}) collective-permute-start(bf16[9,64,128]{2,1,0:T(8,128)(2,1)S(1)} %pad_maximum_fusion.1), channel_id=1, source_target_pairs={{0,8},{8,0},{16,24},{24,16},{1,9},{9,1},{17,25},{25,17},{2,10},{10... | collective-permute-start | bytes 442376 | tf_op jit(solution)/shard_map/ppermute | solution.py:38
  49.1 0.8 collective-permute-done.22.refs_8_
  50.1 1.1 %shard_map.65 = (f32[8,64,128]{2,1,0:T(8,128)S(1)}, bf16[512,128]{1,0:T(8,128)(2,1)S(1)}, bf16[512,128]{1,0:T(8,128)(2,1)S(1)}, bf16[512,128]{1,0:T(8,128)(2,1)S(1)}) custom-call(s32[3,32]{1,0:T(4,128)S(1)} %get-tuple-element.39.refs_0_.refs_1_, bf16[32,128,128]{2,1,0:T(8,128)(2,1)S(1)} %bitcast.8, ...), custom_call_target="tpu_custom_call" | custom-call | flops 67108864 | bytes 2097536 | tf_op jit(solution)/shard_map/pallas_call | solution.py:25
  51.5 1.5 %shard_map.66 = (f32[4,8,64,128]{3,2,1,0:T(8,128)S(1)}, bf16[4,512,128]{2,1,0:T(8,128)(2,1)S(1)}) custom-call(f32[8,64,128]{2,1,0:T(8,128)S(1)} %get-tuple-element.59.refs_0_.refs_4_, s32[3,32]{1,0:T(4,128)S(1)} %get-tuple-element.39.refs_0_.refs_1_, bf16[32,128,128]{2,1,0:T(8,128)(2,1)S(1)} %bitcast.9, ...), custom_call_target="tpu_custom_call" | custom-call | flops 67108864 | bytes 1573248 | tf_op jit(solution)/shard_map/pallas_call | solution.py:25
  53.2 1.7 %collective-permute-start.31 = (bf16[512,128]{1,0:T(8,128)(2,1)S(1)}, bf16[512,128]{1,0:T(8,128)(2,1)S(1)}, u32[]{:S(2)}, u32[]{:S(2)}) collective-permute-start(bf16[512,128]{1,0:T(8,128)(2,1)S(1)} %get-tuple-element.68), channel_id=1, source_target_pairs={{0,8},{8,0},{16,24},{24,16},{1,9},{9,1},{17,25},{25,17},{2,10},{10... | collective-permute-start | bytes 393224 | tf_op jit(solution)/shard_map/ppermute | solution.py:38
  55.6 2.0 %collective-permute-start.33 = (bf16[512,128]{1,0:T(8,128)(2,1)S(1)}, bf16[512,128]{1,0:T(8,128)(2,1)S(1)}, u32[]{:S(2)}, u32[]{:S(2)}) collective-permute-start(bf16[512,128]{1,0:T(8,128)(2,1)S(1)} %get-tuple-element.70), channel_id=1, source_target_pairs={{0,24},{8,16},{16,8},{24,0},{1,25},{9,17},{17,9},{25,1},{2,26},{10... | collective-permute-start | bytes 393224 | tf_op jit(solution)/shard_map/ppermute | solution.py:38
  57.7 1.6 %collective-permute-start.28 = (bf16[512,128]{1,0:T(8,128)(2,1)S(1)}, bf16[512,128]{1,0:T(8,128)(2,1)S(1)}, u32[]{:S(2)}, u32[]{:S(2)}) collective-permute-start(bf16[512,128]{1,0:T(8,128)(2,1)S(1)} %get-tuple-element.65), channel_id=1, source_target_pairs={{0,2},{1,3},{2,0},{3,1},{4,6},{5,7},{6,4},{7,5},{8,10},{9,11},{10,... | collective-permute-start | bytes 393224 | tf_op jit(solution)/shard_map/ppermute | solution.py:38
  59.3 1.5 %collective-permute-start.29 = (bf16[512,128]{1,0:T(8,128)(2,1)S(1)}, bf16[512,128]{1,0:T(8,128)(2,1)S(1)}, u32[]{:S(2)}, u32[]{:S(2)}) collective-permute-start(bf16[512,128]{1,0:T(8,128)(2,1)S(1)} %get-tuple-element.66), channel_id=1, source_target_pairs={{0,4},{1,5},{2,6},{3,7},{4,0},{5,1},{6,2},{7,3},{8,12},{9,13},{10,... | collective-permute-start | bytes 393224 | tf_op jit(solution)/shard_map/ppermute | solution.py:38
  60.8 2.3 %collective-permute-start.30 = (bf16[512,128]{1,0:T(8,128)(2,1)S(1)}, bf16[512,128]{1,0:T(8,128)(2,1)S(1)}, u32[]{:S(2)}, u32[]{:S(2)}) collective-permute-start(bf16[512,128]{1,0:T(8,128)(2,1)S(1)} %get-tuple-element.67), channel_id=1, source_target_pairs={{0,6},{1,7},{2,4},{3,5},{4,2},{5,3},{6,0},{7,1},{8,14},{9,15},{10,... | collective-permute-start | bytes 393224 | tf_op jit(solution)/shard_map/ppermute | solution.py:38
  63.1 4.7 %collective-permute-done.32.refs_9_ = bf16[512,128]{1,0:T(8,128)(2,1)S(1)} collective-permute-done((bf16[512,128]{1,0:T(8,128)(2,1)S(1)}, bf16[512,128]{1,0:T(8,128)(2,1)S(1)}, u32[]{:S(2)}, u32[]{:S(2)}) %collective-permute-start.32) | collective-permute-done | bytes 131104 | tf_op jit(solution)/shard_map/ppermute | solution.py:38
  68.6 2.7 %collective-permute-start.42 = (bf16[8,64,128]{2,1,0:T(8,128)(2,1)S(1)}, bf16[8,64,128]{2,1,0:T(8,128)(2,1)S(1)}, u32[]{:S(2)}, u32[]{:S(2)}) collective-permute-start(bf16[8,64,128]{2,1,0:T(8,128)(2,1)S(1)} %get-tuple-element.72.refs_2_.refs_3_), channel_id=1, source_target_pairs={{0,16},{8,24},{16,0},{24,8},{1,17},{9,25},{17,1},{25,9},{2,18},{10... | collective-permute-start | bytes 393224 | tf_op jit(solution)/shard_map/ppermute | solution.py:38
  71.4 1.8 %collective-permute-start.36 = (bf16[8,64,128]{2,1,0:T(8,128)(2,1)S(1)}, bf16[8,64,128]{2,1,0:T(8,128)(2,1)S(1)}, u32[]{:S(2)}, u32[]{:S(2)}) collective-permute-start(bf16[8,64,128]{2,1,0:T(8,128)(2,1)S(1)} %get-tuple-element.72.refs_2_.refs_3_), channel_id=1, source_target_pairs={{0,6},{1,7},{2,4},{3,5},{4,2},{5,3},{6,0},{7,1},{8,14},{9,15},{10,... | collective-permute-start | bytes 393224 | tf_op jit(solution)/shard_map/ppermute | solution.py:38
  73.2 1.2 %collective-permute-start.35 = (bf16[8,64,128]{2,1,0:T(8,128)(2,1)S(1)}, bf16[8,64,128]{2,1,0:T(8,128)(2,1)S(1)}, u32[]{:S(2)}, u32[]{:S(2)}) collective-permute-start(bf16[8,64,128]{2,1,0:T(8,128)(2,1)S(1)} %get-tuple-element.72.refs_2_.refs_3_), channel_id=1, source_target_pairs={{0,4},{1,5},{2,6},{3,7},{4,0},{5,1},{6,2},{7,3},{8,12},{9,13},{10,... | collective-permute-start | bytes 393224 | tf_op jit(solution)/shard_map/ppermute | solution.py:38
  75.0 2.0 %collective-permute-done.41.refs_5_ = bf16[7,64,128]{2,1,0:T(8,128)(2,1)S(1)} collective-permute-done((bf16[7,64,128]{2,1,0:T(8,128)(2,1)S(1)}, bf16[7,64,128]{2,1,0:T(8,128)(2,1)S(1)}, u32[]{:S(2)}, u32[]{:S(2)}) %collective-permute-start.41) | collective-permute-done | bytes 114720 | tf_op jit(solution)/shard_map/ppermute | solution.py:38
  77.2 1.1 %collective-permute-start.43 = (bf16[9,64,128]{2,1,0:T(8,128)(2,1)S(1)}, bf16[9,64,128]{2,1,0:T(8,128)(2,1)S(1)}, u32[]{:S(2)}, u32[]{:S(2)}) collective-permute-start(bf16[9,64,128]{2,1,0:T(8,128)(2,1)S(1)} %pad_maximum_fusion.2), channel_id=1, source_target_pairs={{0,8},{8,0},{16,24},{24,16},{1,9},{9,1},{17,25},{25,17},{2,10},{10... | collective-permute-start | bytes 442376 | tf_op jit(solution)/shard_map/ppermute | solution.py:38
  80.9 1.0 shard_map.69.refs_1_
  82.4 1.2 %shard_map.70 = f32[40,128]{1,0:T(8,128)S(1)} custom-call(s32[3,32]{1,0:T(4,128)S(1)} %get-tuple-element.39.refs_0_.refs_1_, bf16[64,4096]{1,0:T(8,128)(2,1)S(1)} %shard_map.69.refs_1_, f32[64,128]{1,0:T(8,128)S(1)} %get-tuple-element.73.refs_2_, bf16[8,64,128]{2,1,0:T(8,128)(2,1)S(1)} %get-tuple-element.72.refs_2_.refs_3_, ...), custom_call_target="tpu_custom_call" | custom-call | flops 33554432 | bytes 1081728 | tf_op jit(solution)/shard_map/pallas_call | solution.py:25
  83.7 1.2 %collective-permute-done.44 = f32[40,128]{1,0:T(8,128)S(1)} collective-permute-done((f32[40,128]{1,0:T(8,128)S(1)}, f32[40,128]{1,0:T(8,128)S(1)}, u32[]{:S(2)}, u32[]{:S(2)}) %collective-permute-start.44) | collective-permute-done | bytes 20512 | tf_op jit(solution)/shard_map/ppermute | solution.py:38
  84.9 1.6 %collective-permute-start.47 = (f32[40,128]{1,0:T(8,128)S(1)}, f32[40,128]{1,0:T(8,128)S(1)}, u32[]{:S(2)}, u32[]{:S(2)}) collective-permute-start(f32[40,128]{1,0:T(8,128)S(1)} %add.12), channel_id=1, source_target_pairs={{0,6},{1,7},{2,4},{3,5},{4,2},{5,3},{6,0},{7,1},{8,14},{9,15},{10,... | collective-permute-start | bytes 61448 | tf_op jit(solution)/shard_map/ppermute | solution.py:38
  86.4 1.3 %collective-permute-start.46 = (f32[40,128]{1,0:T(8,128)S(1)}, f32[40,128]{1,0:T(8,128)S(1)}, u32[]{:S(2)}, u32[]{:S(2)}) collective-permute-start(f32[40,128]{1,0:T(8,128)S(1)} %add.12), channel_id=1, source_target_pairs={{0,4},{1,5},{2,6},{3,7},{4,0},{5,1},{6,2},{7,3},{8,12},{9,13},{10,... | collective-permute-start | bytes 61448 | tf_op jit(solution)/shard_map/ppermute | solution.py:38
  88.4 1.2 %collective-permute-done.47 = f32[40,128]{1,0:T(8,128)S(1)} collective-permute-done((f32[40,128]{1,0:T(8,128)S(1)}, f32[40,128]{1,0:T(8,128)S(1)}, u32[]{:S(2)}, u32[]{:S(2)}) %collective-permute-start.47) | collective-permute-done | bytes 20512 | tf_op jit(solution)/shard_map/ppermute | solution.py:38
  90.2 1.3 %collective-permute-done.45 = f32[40,128]{1,0:T(8,128)S(1)} collective-permute-done((f32[40,128]{1,0:T(8,128)S(1)}, f32[40,128]{1,0:T(8,128)S(1)}, u32[]{:S(2)}, u32[]{:S(2)}) %collective-permute-start.45) | collective-permute-done | bytes 20512 | tf_op jit(solution)/shard_map/ppermute | solution.py:38
  91.6 1.9 %collective-permute-start.50 = (f32[40,128]{1,0:T(8,128)S(1)}, f32[40,128]{1,0:T(8,128)S(1)}, u32[]{:S(2)}, u32[]{:S(2)}) collective-permute-start(f32[40,128]{1,0:T(8,128)S(1)} %add_add_fusion.refs_1_), channel_id=1, source_target_pairs={{0,24},{8,16},{16,8},{24,0},{1,25},{9,17},{17,9},{25,1},{2,26},{10... | collective-permute-start | bytes 61448 | tf_op jit(solution)/shard_map/ppermute | solution.py:38
  93.5 0.9 collective-permute-start.49
  94.3 1.7 %collective-permute-start.48 = (f32[40,128]{1,0:T(8,128)S(1)}, f32[40,128]{1,0:T(8,128)S(1)}, u32[]{:S(2)}, u32[]{:S(2)}) collective-permute-start(f32[40,128]{1,0:T(8,128)S(1)} %add_add_fusion.refs_1_), channel_id=1, source_target_pairs={{0,8},{8,0},{16,24},{24,16},{1,9},{9,1},{17,25},{25,17},{2,10},{10... | collective-permute-start | bytes 61448 | tf_op jit(solution)/shard_map/ppermute | solution.py:38
  96.0 1.2 %collective-permute-done.50.refs_4_ = f32[40,128]{1,0:T(8,128)S(1)} collective-permute-done((f32[40,128]{1,0:T(8,128)S(1)}, f32[40,128]{1,0:T(8,128)S(1)}, u32[]{:S(2)}, u32[]{:S(2)}) %collective-permute-start.50) | collective-permute-done | bytes 20512 | tf_op jit(solution)/shard_map/ppermute | solution.py:38
  97.2 1.1 %collective-permute-done.49.refs_3_ = f32[40,128]{1,0:T(8,128)S(1)} collective-permute-done((f32[40,128]{1,0:T(8,128)S(1)}, f32[40,128]{1,0:T(8,128)S(1)}, u32[]{:S(2)}, u32[]{:S(2)}) %collective-permute-start.49) | collective-permute-done | bytes 20512 | tf_op jit(solution)/shard_map/ppermute | solution.py:38
  98.4 7.1 %shard_map.71 = (f32[64,1024]{1,0:T(8,128)}, f32[64,64]{1,0:T(8,128)}) custom-call(f32[64,1024]{1,0:T(8,128)S(1)} %get-tuple-element.71.refs_0_, f32[40,128]{1,0:T(8,128)S(1)} %add_add_fusion.refs_1_, f32[40,128]{1,0:T(8,128)S(1)} %collective-permute-done.48.refs_2_, f32[40,128]{1,0:T(8,128)S(1)} %collective-permute-done.49.refs_3_, ...), custom_call_target="tpu_custom_call" | custom-call | bytes 344064 | tf_op jit(solution)/shard_map/pallas_call | solution.py:25
  (91 shorter events, 16.0 us)
Async XLA Ops:
  2.9 10.6 %collective-permute-start.8 = (bf16[8,64,128]{2,1,0:T(8,128)(2,1)S(1)}, bf16[8,64,128]{2,1,0:T(8,128)(2,1)S(1)}, u32[]{:S(2)}, u32[]{:S(2)}) collective-permute-start(bf16[8,64,128]{2,1,0:T(8,128)(2,1)S(1)} %get-tuple-element.40.refs_2_.refs_3_), channel_id=1, source_target_pairs={{0,16},{8,24},{16,0},{24,8},{1,17},{9,25},{17,1},{25,9},{2,18},{10... | collective-permute-start | bytes 393224 | tf_op jit(solution)/shard_map/ppermute | solution.py:38
  7.0 6.5 %collective-permute-start.7 = (bf16[7,64,128]{2,1,0:T(8,128)(2,1)S(1)}, bf16[7,64,128]{2,1,0:T(8,128)(2,1)S(1)}, u32[]{:S(2)}, u32[]{:S(2)}) collective-permute-start(bf16[7,64,128]{2,1,0:T(8,128)(2,1)S(1)} %slice.18), channel_id=1, source_target_pairs={{0,8},{8,0},{16,24},{24,16},{1,9},{9,1},{17,25},{25,17},{2,10},{10... | collective-permute-start | bytes 344072 | tf_op jit(solution)/shard_map/ppermute | solution.py:38
  8.7 6.6 %collective-permute-start.2 = (bf16[8,64,128]{2,1,0:T(8,128)(2,1)S(1)}, bf16[8,64,128]{2,1,0:T(8,128)(2,1)S(1)}, u32[]{:S(2)}, u32[]{:S(2)}) collective-permute-start(bf16[8,64,128]{2,1,0:T(8,128)(2,1)S(1)} %get-tuple-element.40.refs_2_.refs_3_), channel_id=1, source_target_pairs={{0,6},{1,7},{2,4},{3,5},{4,2},{5,3},{6,0},{7,1},{8,14},{9,15},{10,... | collective-permute-start | bytes 393224 | tf_op jit(solution)/shard_map/ppermute | solution.py:38
  11.1 5.9 %collective-permute-start.1 = (bf16[8,64,128]{2,1,0:T(8,128)(2,1)S(1)}, bf16[8,64,128]{2,1,0:T(8,128)(2,1)S(1)}, u32[]{:S(2)}, u32[]{:S(2)}) collective-permute-start(bf16[8,64,128]{2,1,0:T(8,128)(2,1)S(1)} %get-tuple-element.40.refs_2_.refs_3_), channel_id=1, source_target_pairs={{0,4},{1,5},{2,6},{3,7},{4,0},{5,1},{6,2},{7,3},{8,12},{9,13},{10,... | collective-permute-start | bytes 393224 | tf_op jit(solution)/shard_map/ppermute | solution.py:38
  11.6 5.5 %collective-permute-start = (bf16[8,64,128]{2,1,0:T(8,128)(2,1)S(1)}, bf16[8,64,128]{2,1,0:T(8,128)(2,1)S(1)}, u32[]{:S(2)}, u32[]{:S(2)}) collective-permute-start(bf16[8,64,128]{2,1,0:T(8,128)(2,1)S(1)} %get-tuple-element.40.refs_2_.refs_3_), channel_id=1, source_target_pairs={{0,2},{1,3},{2,0},{3,1},{4,6},{5,7},{6,4},{7,5},{8,10},{9,11},{10,... | collective-permute-start | bytes 393224 | tf_op jit(solution)/shard_map/ppermute | solution.py:38
  13.5 8.0 %collective-permute-start.9 = (bf16[9,64,128]{2,1,0:T(8,128)(2,1)S(1)}, bf16[9,64,128]{2,1,0:T(8,128)(2,1)S(1)}, u32[]{:S(2)}, u32[]{:S(2)}) collective-permute-start(bf16[9,64,128]{2,1,0:T(8,128)(2,1)S(1)} %pad_maximum_fusion), channel_id=1, source_target_pairs={{0,8},{8,0},{16,24},{24,16},{1,9},{9,1},{17,25},{25,17},{2,10},{10... | collective-permute-start | bytes 442376 | tf_op jit(solution)/shard_map/ppermute | solution.py:38
  14.8 5.5 %collective-permute-start.3 = (bf16[8,64,128]{2,1,0:T(8,128)(2,1)S(1)}, bf16[8,64,128]{2,1,0:T(8,128)(2,1)S(1)}, u32[]{:S(2)}, u32[]{:S(2)}) collective-permute-start(bf16[8,64,128]{2,1,0:T(8,128)(2,1)S(1)} %get-tuple-element.40.refs_2_.refs_3_), channel_id=1, source_target_pairs={{0,1},{1,0},{2,3},{3,2},{4,5},{5,4},{6,7},{7,6},{8,9},{9,8},{10,11... | collective-permute-start | bytes 393224 | tf_op jit(solution)/shard_map/ppermute | solution.py:38
  15.2 5.1 %collective-permute-start.6 = (bf16[8,64,128]{2,1,0:T(8,128)(2,1)S(1)}, bf16[8,64,128]{2,1,0:T(8,128)(2,1)S(1)}, u32[]{:S(2)}, u32[]{:S(2)}) collective-permute-start(bf16[8,64,128]{2,1,0:T(8,128)(2,1)S(1)} %collective-permute-done.2.refs_5_), channel_id=1, source_target_pairs={{0,1},{1,0},{2,3},{3,2},{4,5},{5,4},{6,7},{7,6},{8,9},{9,8},{10,11... | collective-permute-start | bytes 393224 | tf_op jit(solution)/shard_map/ppermute | solution.py:38
  17.0 3.3 %collective-permute-start.5 = (bf16[8,64,128]{2,1,0:T(8,128)(2,1)S(1)}, bf16[8,64,128]{2,1,0:T(8,128)(2,1)S(1)}, u32[]{:S(2)}, u32[]{:S(2)}) collective-permute-start(bf16[8,64,128]{2,1,0:T(8,128)(2,1)S(1)} %collective-permute-done.1.refs_4_), channel_id=1, source_target_pairs={{0,1},{1,0},{2,3},{3,2},{4,5},{5,4},{6,7},{7,6},{8,9},{9,8},{10,11... | collective-permute-start | bytes 393224 | tf_op jit(solution)/shard_map/ppermute | solution.py:38
  17.1 3.2 %collective-permute-start.4 = (bf16[8,64,128]{2,1,0:T(8,128)(2,1)S(1)}, bf16[8,64,128]{2,1,0:T(8,128)(2,1)S(1)}, u32[]{:S(2)}, u32[]{:S(2)}) collective-permute-start(bf16[8,64,128]{2,1,0:T(8,128)(2,1)S(1)} %collective-permute-done.refs_3_), channel_id=1, source_target_pairs={{0,1},{1,0},{2,3},{3,2},{4,5},{5,4},{6,7},{7,6},{8,9},{9,8},{10,11... | collective-permute-start | bytes 393224 | tf_op jit(solution)/shard_map/ppermute | solution.py:38
  23.0 4.5 %collective-permute-start.10 = (bf16[4,528,128]{2,1,0:T(8,128)(2,1)S(1)}, bf16[4,528,128]{2,1,0:T(8,128)(2,1)S(1)}, u32[]{:S(2)}, u32[]{:S(2)}) collective-permute-start(bf16[4,528,128]{2,1,0:T(8,128)(2,1)S(1)} %get-tuple-element.47), channel_id=1, source_target_pairs={{0,1},{1,0},{2,3},{3,2},{4,5},{5,4},{6,7},{7,6},{8,9},{9,8},{10,11... | collective-permute-start | bytes 1622024 | tf_op jit(solution)/shard_map/ppermute | solution.py:38
  23.2 8.1 %collective-permute-start.14 = (bf16[528,128]{1,0:T(8,128)(2,1)S(1)}, bf16[528,128]{1,0:T(8,128)(2,1)S(1)}, u32[]{:S(2)}, u32[]{:S(2)}) collective-permute-start(bf16[528,128]{1,0:T(8,128)(2,1)S(1)} %get-tuple-element.53), channel_id=1, source_target_pairs={{0,8},{8,0},{16,24},{24,16},{1,9},{9,1},{17,25},{25,17},{2,10},{10... | collective-permute-start | bytes 405512 | tf_op jit(solution)/shard_map/ppermute | solution.py:38
  23.6 13.2 %collective-permute-start.15 = (bf16[528,128]{1,0:T(8,128)(2,1)S(1)}, bf16[528,128]{1,0:T(8,128)(2,1)S(1)}, u32[]{:S(2)}, u32[]{:S(2)}) collective-permute-start(bf16[528,128]{1,0:T(8,128)(2,1)S(1)} %get-tuple-element.54), channel_id=1, source_target_pairs={{0,16},{8,24},{16,0},{24,8},{1,17},{9,25},{17,1},{25,9},{2,18},{10... | collective-permute-start | bytes 405512 | tf_op jit(solution)/shard_map/ppermute | solution.py:38
  24.9 11.9 %collective-permute-start.16 = (bf16[528,128]{1,0:T(8,128)(2,1)S(1)}, bf16[528,128]{1,0:T(8,128)(2,1)S(1)}, u32[]{:S(2)}, u32[]{:S(2)}) collective-permute-start(bf16[528,128]{1,0:T(8,128)(2,1)S(1)} %get-tuple-element.55), channel_id=1, source_target_pairs={{0,24},{8,16},{16,8},{24,0},{1,25},{9,17},{17,9},{25,1},{2,26},{10... | collective-permute-start | bytes 405512 | tf_op jit(solution)/shard_map/ppermute | solution.py:38
  27.7 9.1 %collective-permute-start.11 = (bf16[528,128]{1,0:T(8,128)(2,1)S(1)}, bf16[528,128]{1,0:T(8,128)(2,1)S(1)}, u32[]{:S(2)}, u32[]{:S(2)}) collective-permute-start(bf16[528,128]{1,0:T(8,128)(2,1)S(1)} %get-tuple-element.50), channel_id=1, source_target_pairs={{0,2},{1,3},{2,0},{3,1},{4,6},{5,7},{6,4},{7,5},{8,10},{9,11},{10,... | collective-permute-start | bytes 405512 | tf_op jit(solution)/shard_map/ppermute | solution.py:38
  29.3 7.5 %collective-permute-start.12 = (bf16[528,128]{1,0:T(8,128)(2,1)S(1)}, bf16[528,128]{1,0:T(8,128)(2,1)S(1)}, u32[]{:S(2)}, u32[]{:S(2)}) collective-permute-start(bf16[528,128]{1,0:T(8,128)(2,1)S(1)} %get-tuple-element.51), channel_id=1, source_target_pairs={{0,4},{1,5},{2,6},{3,7},{4,0},{5,1},{6,2},{7,3},{8,12},{9,13},{10,... | collective-permute-start | bytes 405512 | tf_op jit(solution)/shard_map/ppermute | solution.py:38
  31.3 6.0 %collective-permute-start.13 = (bf16[528,128]{1,0:T(8,128)(2,1)S(1)}, bf16[528,128]{1,0:T(8,128)(2,1)S(1)}, u32[]{:S(2)}, u32[]{:S(2)}) collective-permute-start(bf16[528,128]{1,0:T(8,128)(2,1)S(1)} %get-tuple-element.52), channel_id=1, source_target_pairs={{0,6},{1,7},{2,4},{3,5},{4,2},{5,3},{6,0},{7,1},{8,14},{9,15},{10,... | collective-permute-start | bytes 405512 | tf_op jit(solution)/shard_map/ppermute | solution.py:38
  37.5 8.7 %collective-permute-start.25 = (bf16[8,64,128]{2,1,0:T(8,128)(2,1)S(1)}, bf16[8,64,128]{2,1,0:T(8,128)(2,1)S(1)}, u32[]{:S(2)}, u32[]{:S(2)}) collective-permute-start(bf16[8,64,128]{2,1,0:T(8,128)(2,1)S(1)} %get-tuple-element.58.refs_2_.refs_3_), channel_id=1, source_target_pairs={{0,16},{8,24},{16,0},{24,8},{1,17},{9,25},{17,1},{25,9},{2,18},{10... | collective-permute-start | bytes 393224 | tf_op jit(solution)/shard_map/ppermute | solution.py:38
  40.3 5.7 %collective-permute-start.24 = (bf16[7,64,128]{2,1,0:T(8,128)(2,1)S(1)}, bf16[7,64,128]{2,1,0:T(8,128)(2,1)S(1)}, u32[]{:S(2)}, u32[]{:S(2)}) collective-permute-start(bf16[7,64,128]{2,1,0:T(8,128)(2,1)S(1)} %slice.20), channel_id=1, source_target_pairs={{0,8},{8,0},{16,24},{24,16},{1,9},{9,1},{17,25},{25,17},{2,10},{10... | collective-permute-start | bytes 344072 | tf_op jit(solution)/shard_map/ppermute | solution.py:38
  40.4 7.2 %collective-permute-start.19 = (bf16[8,64,128]{2,1,0:T(8,128)(2,1)S(1)}, bf16[8,64,128]{2,1,0:T(8,128)(2,1)S(1)}, u32[]{:S(2)}, u32[]{:S(2)}) collective-permute-start(bf16[8,64,128]{2,1,0:T(8,128)(2,1)S(1)} %get-tuple-element.58.refs_2_.refs_3_), channel_id=1, source_target_pairs={{0,6},{1,7},{2,4},{3,5},{4,2},{5,3},{6,0},{7,1},{8,14},{9,15},{10,... | collective-permute-start | bytes 393224 | tf_op jit(solution)/shard_map/ppermute | solution.py:38
  42.8 5.8 %collective-permute-start.18 = (bf16[8,64,128]{2,1,0:T(8,128)(2,1)S(1)}, bf16[8,64,128]{2,1,0:T(8,128)(2,1)S(1)}, u32[]{:S(2)}, u32[]{:S(2)}) collective-permute-start(bf16[8,64,128]{2,1,0:T(8,128)(2,1)S(1)} %get-tuple-element.58.refs_2_.refs_3_), channel_id=1, source_target_pairs={{0,4},{1,5},{2,6},{3,7},{4,0},{5,1},{6,2},{7,3},{8,12},{9,13},{10,... | collective-permute-start | bytes 393224 | tf_op jit(solution)/shard_map/ppermute | solution.py:38
  43.4 5.3 %collective-permute-start.17 = (bf16[8,64,128]{2,1,0:T(8,128)(2,1)S(1)}, bf16[8,64,128]{2,1,0:T(8,128)(2,1)S(1)}, u32[]{:S(2)}, u32[]{:S(2)}) collective-permute-start(bf16[8,64,128]{2,1,0:T(8,128)(2,1)S(1)} %get-tuple-element.58.refs_2_.refs_3_), channel_id=1, source_target_pairs={{0,2},{1,3},{2,0},{3,1},{4,6},{5,7},{6,4},{7,5},{8,10},{9,11},{10,... | collective-permute-start | bytes 393224 | tf_op jit(solution)/shard_map/ppermute | solution.py:38
  46.3 5.2 %collective-permute-start.26 = (bf16[9,64,128]{2,1,0:T(8,128)(2,1)S(1)}, bf16[9,64,128]{2,1,0:T(8,128)(2,1)S(1)}, u32[]{:S(2)}, u32[]{:S(2)}) collective-permute-start(bf16[9,64,128]{2,1,0:T(8,128)(2,1)S(1)} %pad_maximum_fusion.1), channel_id=1, source_target_pairs={{0,8},{8,0},{16,24},{24,16},{1,9},{9,1},{17,25},{25,17},{2,10},{10... | collective-permute-start | bytes 442376 | tf_op jit(solution)/shard_map/ppermute | solution.py:38
  47.6 1.5 %collective-permute-start.20 = (bf16[8,64,128]{2,1,0:T(8,128)(2,1)S(1)}, bf16[8,64,128]{2,1,0:T(8,128)(2,1)S(1)}, u32[]{:S(2)}, u32[]{:S(2)}) collective-permute-start(bf16[8,64,128]{2,1,0:T(8,128)(2,1)S(1)} %get-tuple-element.58.refs_2_.refs_3_), channel_id=1, source_target_pairs={{0,1},{1,0},{2,3},{3,2},{4,5},{5,4},{6,7},{7,6},{8,9},{9,8},{10,11... | collective-permute-start | bytes 393224 | tf_op jit(solution)/shard_map/ppermute | solution.py:38
  47.6 1.5 %collective-permute-start.23 = (bf16[8,64,128]{2,1,0:T(8,128)(2,1)S(1)}, bf16[8,64,128]{2,1,0:T(8,128)(2,1)S(1)}, u32[]{:S(2)}, u32[]{:S(2)}) collective-permute-start(bf16[8,64,128]{2,1,0:T(8,128)(2,1)S(1)} %collective-permute-done.19.refs_5_), channel_id=1, source_target_pairs={{0,1},{1,0},{2,3},{3,2},{4,5},{5,4},{6,7},{7,6},{8,9},{9,8},{10,11... | collective-permute-start | bytes 393224 | tf_op jit(solution)/shard_map/ppermute | solution.py:38
  48.6 1.3 %collective-permute-start.22 = (bf16[8,64,128]{2,1,0:T(8,128)(2,1)S(1)}, bf16[8,64,128]{2,1,0:T(8,128)(2,1)S(1)}, u32[]{:S(2)}, u32[]{:S(2)}) collective-permute-start(bf16[8,64,128]{2,1,0:T(8,128)(2,1)S(1)} %collective-permute-done.18.refs_4_), channel_id=1, source_target_pairs={{0,1},{1,0},{2,3},{3,2},{4,5},{5,4},{6,7},{7,6},{8,9},{9,8},{10,11... | collective-permute-start | bytes 393224 | tf_op jit(solution)/shard_map/ppermute | solution.py:38
  48.7 1.5 %collective-permute-start.21 = (bf16[8,64,128]{2,1,0:T(8,128)(2,1)S(1)}, bf16[8,64,128]{2,1,0:T(8,128)(2,1)S(1)}, u32[]{:S(2)}, u32[]{:S(2)}) collective-permute-start(bf16[8,64,128]{2,1,0:T(8,128)(2,1)S(1)} %collective-permute-done.17.refs_3_), channel_id=1, source_target_pairs={{0,1},{1,0},{2,3},{3,2},{4,5},{5,4},{6,7},{7,6},{8,9},{9,8},{10,11... | collective-permute-start | bytes 393224 | tf_op jit(solution)/shard_map/ppermute | solution.py:38
  53.0 4.6 %collective-permute-start.27 = (bf16[4,512,128]{2,1,0:T(8,128)(2,1)S(1)}, bf16[4,512,128]{2,1,0:T(8,128)(2,1)S(1)}, u32[]{:S(2)}, u32[]{:S(2)}) collective-permute-start(bf16[4,512,128]{2,1,0:T(8,128)(2,1)S(1)} %get-tuple-element.63), channel_id=1, source_target_pairs={{0,1},{1,0},{2,3},{3,2},{4,5},{5,4},{6,7},{7,6},{8,9},{9,8},{10,11... | collective-permute-start | bytes 1572872 | tf_op jit(solution)/shard_map/ppermute | solution.py:38
  53.2 7.6 %collective-permute-start.31 = (bf16[512,128]{1,0:T(8,128)(2,1)S(1)}, bf16[512,128]{1,0:T(8,128)(2,1)S(1)}, u32[]{:S(2)}, u32[]{:S(2)}) collective-permute-start(bf16[512,128]{1,0:T(8,128)(2,1)S(1)} %get-tuple-element.68), channel_id=1, source_target_pairs={{0,8},{8,0},{16,24},{24,16},{1,9},{9,1},{17,25},{25,17},{2,10},{10... | collective-permute-start | bytes 393224 | tf_op jit(solution)/shard_map/ppermute | solution.py:38
  54.9 12.9 %collective-permute-start.32 = (bf16[512,128]{1,0:T(8,128)(2,1)S(1)}, bf16[512,128]{1,0:T(8,128)(2,1)S(1)}, u32[]{:S(2)}, u32[]{:S(2)}) collective-permute-start(bf16[512,128]{1,0:T(8,128)(2,1)S(1)} %get-tuple-element.69), channel_id=1, source_target_pairs={{0,16},{8,24},{16,0},{24,8},{1,17},{9,25},{17,1},{25,9},{2,18},{10... | collective-permute-start | bytes 393224 | tf_op jit(solution)/shard_map/ppermute | solution.py:38
  55.6 12.2 %collective-permute-start.33 = (bf16[512,128]{1,0:T(8,128)(2,1)S(1)}, bf16[512,128]{1,0:T(8,128)(2,1)S(1)}, u32[]{:S(2)}, u32[]{:S(2)}) collective-permute-start(bf16[512,128]{1,0:T(8,128)(2,1)S(1)} %get-tuple-element.70), channel_id=1, source_target_pairs={{0,24},{8,16},{16,8},{24,0},{1,25},{9,17},{17,9},{25,1},{2,26},{10... | collective-permute-start | bytes 393224 | tf_op jit(solution)/shard_map/ppermute | solution.py:38
  57.7 10.1 %collective-permute-start.28 = (bf16[512,128]{1,0:T(8,128)(2,1)S(1)}, bf16[512,128]{1,0:T(8,128)(2,1)S(1)}, u32[]{:S(2)}, u32[]{:S(2)}) collective-permute-start(bf16[512,128]{1,0:T(8,128)(2,1)S(1)} %get-tuple-element.65), channel_id=1, source_target_pairs={{0,2},{1,3},{2,0},{3,1},{4,6},{5,7},{6,4},{7,5},{8,10},{9,11},{10,... | collective-permute-start | bytes 393224 | tf_op jit(solution)/shard_map/ppermute | solution.py:38
  59.3 8.5 %collective-permute-start.29 = (bf16[512,128]{1,0:T(8,128)(2,1)S(1)}, bf16[512,128]{1,0:T(8,128)(2,1)S(1)}, u32[]{:S(2)}, u32[]{:S(2)}) collective-permute-start(bf16[512,128]{1,0:T(8,128)(2,1)S(1)} %get-tuple-element.66), channel_id=1, source_target_pairs={{0,4},{1,5},{2,6},{3,7},{4,0},{5,1},{6,2},{7,3},{8,12},{9,13},{10,... | collective-permute-start | bytes 393224 | tf_op jit(solution)/shard_map/ppermute | solution.py:38
  60.8 7.0 %collective-permute-start.30 = (bf16[512,128]{1,0:T(8,128)(2,1)S(1)}, bf16[512,128]{1,0:T(8,128)(2,1)S(1)}, u32[]{:S(2)}, u32[]{:S(2)}) collective-permute-start(bf16[512,128]{1,0:T(8,128)(2,1)S(1)} %get-tuple-element.67), channel_id=1, source_target_pairs={{0,6},{1,7},{2,4},{3,5},{4,2},{5,3},{6,0},{7,1},{8,14},{9,15},{10,... | collective-permute-start | bytes 393224 | tf_op jit(solution)/shard_map/ppermute | solution.py:38
  68.6 8.6 %collective-permute-start.42 = (bf16[8,64,128]{2,1,0:T(8,128)(2,1)S(1)}, bf16[8,64,128]{2,1,0:T(8,128)(2,1)S(1)}, u32[]{:S(2)}, u32[]{:S(2)}) collective-permute-start(bf16[8,64,128]{2,1,0:T(8,128)(2,1)S(1)} %get-tuple-element.72.refs_2_.refs_3_), channel_id=1, source_target_pairs={{0,16},{8,24},{16,0},{24,8},{1,17},{9,25},{17,1},{25,9},{2,18},{10... | collective-permute-start | bytes 393224 | tf_op jit(solution)/shard_map/ppermute | solution.py:38
  71.3 5.6 %collective-permute-start.41 = (bf16[7,64,128]{2,1,0:T(8,128)(2,1)S(1)}, bf16[7,64,128]{2,1,0:T(8,128)(2,1)S(1)}, u32[]{:S(2)}, u32[]{:S(2)}) collective-permute-start(bf16[7,64,128]{2,1,0:T(8,128)(2,1)S(1)} %slice.22), channel_id=1, source_target_pairs={{0,8},{8,0},{16,24},{24,16},{1,9},{9,1},{17,25},{25,17},{2,10},{10... | collective-permute-start | bytes 344072 | tf_op jit(solution)/shard_map/ppermute | solution.py:38
  71.4 7.3 %collective-permute-start.36 = (bf16[8,64,128]{2,1,0:T(8,128)(2,1)S(1)}, bf16[8,64,128]{2,1,0:T(8,128)(2,1)S(1)}, u32[]{:S(2)}, u32[]{:S(2)}) collective-permute-start(bf16[8,64,128]{2,1,0:T(8,128)(2,1)S(1)} %get-tuple-element.72.refs_2_.refs_3_), channel_id=1, source_target_pairs={{0,6},{1,7},{2,4},{3,5},{4,2},{5,3},{6,0},{7,1},{8,14},{9,15},{10,... | collective-permute-start | bytes 393224 | tf_op jit(solution)/shard_map/ppermute | solution.py:38
  73.2 6.1 %collective-permute-start.35 = (bf16[8,64,128]{2,1,0:T(8,128)(2,1)S(1)}, bf16[8,64,128]{2,1,0:T(8,128)(2,1)S(1)}, u32[]{:S(2)}, u32[]{:S(2)}) collective-permute-start(bf16[8,64,128]{2,1,0:T(8,128)(2,1)S(1)} %get-tuple-element.72.refs_2_.refs_3_), channel_id=1, source_target_pairs={{0,4},{1,5},{2,6},{3,7},{4,0},{5,1},{6,2},{7,3},{8,12},{9,13},{10,... | collective-permute-start | bytes 393224 | tf_op jit(solution)/shard_map/ppermute | solution.py:38
  74.4 5.1 %collective-permute-start.34 = (bf16[8,64,128]{2,1,0:T(8,128)(2,1)S(1)}, bf16[8,64,128]{2,1,0:T(8,128)(2,1)S(1)}, u32[]{:S(2)}, u32[]{:S(2)}) collective-permute-start(bf16[8,64,128]{2,1,0:T(8,128)(2,1)S(1)} %get-tuple-element.72.refs_2_.refs_3_), channel_id=1, source_target_pairs={{0,2},{1,3},{2,0},{3,1},{4,6},{5,7},{6,4},{7,5},{8,10},{9,11},{10,... | collective-permute-start | bytes 393224 | tf_op jit(solution)/shard_map/ppermute | solution.py:38
  77.2 5.2 %collective-permute-start.43 = (bf16[9,64,128]{2,1,0:T(8,128)(2,1)S(1)}, bf16[9,64,128]{2,1,0:T(8,128)(2,1)S(1)}, u32[]{:S(2)}, u32[]{:S(2)}) collective-permute-start(bf16[9,64,128]{2,1,0:T(8,128)(2,1)S(1)} %pad_maximum_fusion.2), channel_id=1, source_target_pairs={{0,8},{8,0},{16,24},{24,16},{1,9},{9,1},{17,25},{25,17},{2,10},{10... | collective-permute-start | bytes 442376 | tf_op jit(solution)/shard_map/ppermute | solution.py:38
  78.3 1.6 %collective-permute-start.37 = (bf16[8,64,128]{2,1,0:T(8,128)(2,1)S(1)}, bf16[8,64,128]{2,1,0:T(8,128)(2,1)S(1)}, u32[]{:S(2)}, u32[]{:S(2)}) collective-permute-start(bf16[8,64,128]{2,1,0:T(8,128)(2,1)S(1)} %get-tuple-element.72.refs_2_.refs_3_), channel_id=1, source_target_pairs={{0,1},{1,0},{2,3},{3,2},{4,5},{5,4},{6,7},{7,6},{8,9},{9,8},{10,11... | collective-permute-start | bytes 393224 | tf_op jit(solution)/shard_map/ppermute | solution.py:38
  79.5 1.5 %collective-permute-start.38 = (bf16[8,64,128]{2,1,0:T(8,128)(2,1)S(1)}, bf16[8,64,128]{2,1,0:T(8,128)(2,1)S(1)}, u32[]{:S(2)}, u32[]{:S(2)}) collective-permute-start(bf16[8,64,128]{2,1,0:T(8,128)(2,1)S(1)} %collective-permute-done.34.refs_3_), channel_id=1, source_target_pairs={{0,1},{1,0},{2,3},{3,2},{4,5},{5,4},{6,7},{7,6},{8,9},{9,8},{10,11... | collective-permute-start | bytes 393224 | tf_op jit(solution)/shard_map/ppermute | solution.py:38
  84.9 4.7 %collective-permute-start.47 = (f32[40,128]{1,0:T(8,128)S(1)}, f32[40,128]{1,0:T(8,128)S(1)}, u32[]{:S(2)}, u32[]{:S(2)}) collective-permute-start(f32[40,128]{1,0:T(8,128)S(1)} %add.12), channel_id=1, source_target_pairs={{0,6},{1,7},{2,4},{3,5},{4,2},{5,3},{6,0},{7,1},{8,14},{9,15},{10,... | collective-permute-start | bytes 61448 | tf_op jit(solution)/shard_map/ppermute | solution.py:38
  86.4 3.8 %collective-permute-start.46 = (f32[40,128]{1,0:T(8,128)S(1)}, f32[40,128]{1,0:T(8,128)S(1)}, u32[]{:S(2)}, u32[]{:S(2)}) collective-permute-start(f32[40,128]{1,0:T(8,128)S(1)} %add.12), channel_id=1, source_target_pairs={{0,4},{1,5},{2,6},{3,7},{4,0},{5,1},{6,2},{7,3},{8,12},{9,13},{10,... | collective-permute-start | bytes 61448 | tf_op jit(solution)/shard_map/ppermute | solution.py:38
  87.8 3.8 %collective-permute-start.45 = (f32[40,128]{1,0:T(8,128)S(1)}, f32[40,128]{1,0:T(8,128)S(1)}, u32[]{:S(2)}, u32[]{:S(2)}) collective-permute-start(f32[40,128]{1,0:T(8,128)S(1)} %add.12), channel_id=1, source_target_pairs={{0,2},{1,3},{2,0},{3,1},{4,6},{5,7},{6,4},{7,5},{8,10},{9,11},{10,... | collective-permute-start | bytes 61448 | tf_op jit(solution)/shard_map/ppermute | solution.py:38
  91.6 5.6 %collective-permute-start.50 = (f32[40,128]{1,0:T(8,128)S(1)}, f32[40,128]{1,0:T(8,128)S(1)}, u32[]{:S(2)}, u32[]{:S(2)}) collective-permute-start(f32[40,128]{1,0:T(8,128)S(1)} %add_add_fusion.refs_1_), channel_id=1, source_target_pairs={{0,24},{8,16},{16,8},{24,0},{1,25},{9,17},{17,9},{25,1},{2,26},{10... | collective-permute-start | bytes 61448 | tf_op jit(solution)/shard_map/ppermute | solution.py:38
  93.5 4.9 %collective-permute-start.49 = (f32[40,128]{1,0:T(8,128)S(1)}, f32[40,128]{1,0:T(8,128)S(1)}, u32[]{:S(2)}, u32[]{:S(2)}) collective-permute-start(f32[40,128]{1,0:T(8,128)S(1)} %add_add_fusion.refs_1_), channel_id=1, source_target_pairs={{0,16},{8,24},{16,0},{24,8},{1,17},{9,25},{17,1},{25,9},{2,18},{10... | collective-permute-start | bytes 61448 | tf_op jit(solution)/shard_map/ppermute | solution.py:38
  94.3 4.0 %collective-permute-start.48 = (f32[40,128]{1,0:T(8,128)S(1)}, f32[40,128]{1,0:T(8,128)S(1)}, u32[]{:S(2)}, u32[]{:S(2)}) collective-permute-start(f32[40,128]{1,0:T(8,128)S(1)} %add_add_fusion.refs_1_), channel_id=1, source_target_pairs={{0,8},{8,0},{16,24},{24,16},{1,9},{9,1},{17,25},{25,17},{2,10},{10... | collective-permute-start | bytes 61448 | tf_op jit(solution)/shard_map/ppermute | solution.py:38
  (9 other events, 18.8 us)

commit v11 on v10

--- a/solution.py
+++ b/solution.py
@@ -273,9 +273,10 @@
     packed = jnp.where(col >= row, gram_ref[:, :vectors_n], projected)
     diagonal = jnp.sum(jnp.where(row == col, projected, 0.0), 0, keepdims=True)
     half = vectors_n // 2
-    out_ref[:half] = jnp.concatenate([packed[:half], packed[half:]], 1)
     diagonal = jnp.broadcast_to(diagonal, (8, vectors_n))
-    out_ref[half:] = jnp.concatenate([diagonal, jnp.zeros_like(diagonal)], 1)
+    for d in range(out_ref.shape[0]):
+        out_ref[d, :half] = jnp.concatenate([packed[:half], packed[half:]], 1)
+        out_ref[d, half:] = jnp.concatenate([diagonal, jnp.zeros_like(diagonal)], 1)
 
 
 def square_index(n):
@@ -287,27 +288,48 @@
     row, col = square_index(n)
     table = jnp.concatenate([gram, jnp.where(row == col, 1.0, 0.0)], 1)
     bands = [table[i : i + 8] for i in range(0, n, 8)]
-    below = lax.broadcasted_iota(jnp.int32, (8, 2 * n), 0)
-    for j in range(n):
-        at, line = j // 8, j % 8
-        lanes = {i: jnp.broadcast_to(bands[i][:, j : j + 1], below.shape) for i in range(at, n // 8)}
-        pivot_row = bands[at][line : line + 1, :] * (1.0 / lanes[at][line : line + 1, :])
-        pivot_row = jnp.broadcast_to(pivot_row, below.shape)
-        for i in range(at, n // 8):
-            update = lanes[i] * pivot_row
-            if i == at:
-                update = jnp.where(below > line, update, 0.0)
+    shape = (8, 2 * n)
+    line = lax.broadcasted_iota(jnp.int32, shape, 0)
+
+    def spread(values, j):
+        return jnp.broadcast_to(values[:, j : j + 1], shape)
+
+    def pick(values, i):
+        return jnp.broadcast_to(values[i : i + 1, :], shape)
+
+    for at in range(n // 8):
+        block = [spread(bands[at], 8 * at + c) for c in range(8)]
+        forward, solved = bands[at], bands[at]
+        solved_block = list(block)
+        for s in range(8):
+            scale = 1.0 / pick(block[s], s)
+            below = jnp.where(line > s, block[s], 0.0) * scale
+            above = jnp.where(line < s, solved_block[s] * scale, 0.0)
+            both = below + above
+            pivot_row = pick(forward, s)
+            forward = forward - below * pivot_row
+            solved = solved - both * pivot_row
+            for c in range(s + 1, 8):
+                pivot = pick(block[c], s)
+                block[c] = block[c] - below * pivot
+                solved_block[c] = solved_block[c] - both * pivot
+        pivots = block[0]
+        for s in range(1, 8):
+            pivots = jnp.where(line == s, block[s], pivots)
+        solved = solved / pivots
+        bands[at] = forward / jnp.sqrt(pivots)
+        for i in range(at + 1, n // 8):
+            update = spread(bands[i], 8 * at) * pick(solved, 0)
+            for c in range(1, 8):
+                update = update + spread(bands[i], 8 * at + c) * pick(solved, c)
             bands[i] = bands[i] - update
-    table = jnp.concatenate(bands, 0)
-    pivots = jnp.sum(jnp.where(row == col, table[:, :n], 0.0), 1, keepdims=True)
-    return table[:, n:] / jnp.sqrt(pivots)
-
-
-def last_kernel(total_nodes, filtered_ref, *refs):
-    parts, (ritz_ref, rayleigh_ref) = refs[:-2], refs[-2:]
+    return jnp.concatenate(bands, 0)[:, n:]
+
+
+def last_kernel(total_nodes, filtered_ref, sums_ref, ritz_ref, rayleigh_ref):
     n = filtered_ref.shape[0]
     half = n // 2
-    sums = tree_sum([part[...] for part in parts]) * (1.0 / total_nodes)
+    sums = jnp.sum(sums_ref[...], 0) * (1.0 / total_nodes)
     packed = jnp.concatenate([sums[:half, :n], sums[:half, n:]], 0)
     row, col = square_index(n)
     upper = jnp.where(col > row, packed, 0.0)
@@ -324,12 +346,6 @@
     rayleigh_ref[...] = dot(half_way, inverse, NT)
     turned = dot(inverse, half_way, NT)
     ritz_ref[...] = dot(turned, dot(inverse, filtered_ref[...], NN), NN)
-
-
-def tree_sum(parts):
-    while len(parts) > 1:
-        parts = [a + b for a, b in zip(parts[::2], parts[1::2])]
-    return parts[0]
 
 
 def local(tiles, tile_rows, tile_cols, start):
@@ -425,21 +441,22 @@
     )
     sums = call(
         functools.partial(form_kernel, runs[0]),
-        jax.ShapeDtypeStruct((vectors_n // 2 + 8, 2 * vectors_n), F32),
+        jax.ShapeDtypeStruct((cols_n, vectors_n // 2 + 8, 2 * vectors_n), F32),
         [pltpu.VMEM((rows_n * group, vectors_n, width), BF16), pltpu.VMEM(spread, BF16)],
         24,
         [table, left, gram, *col_parts],
         2 * vectors_n * spread[0] * spread[1],
         1,
     )
-    sums = sums + trade(sums, "col", 1)
-    sums = tree_sum([sums, *exchange([sums] * (chips_n - 1), "col", 2)])
+    sums = jnp.sum(lax.all_to_all(sums, "col", 0, 0, tiled=True), 0)
+    sums = jnp.broadcast_to(sums, (rows_n, *sums.shape))
+    sums = lax.all_to_all(sums, "row", 0, 0, tiled=True)
     return call(
         functools.partial(last_kernel, total_nodes),
         [vector_shape, jax.ShapeDtypeStruct((vectors_n, vectors_n), F32)],
         [],
         24,
-        [filtered, sums, *exchange([sums] * (rows_n - 1), "row")],
+        [filtered, sums],
     )
 
 

time: 106 us -> 106 us (level)
  blocking collectives: 0 us -> 18.3 us
  starting transfers between devices: 54.7 us -> 46.7 us
  waiting for transfers between devices: 29 us -> 22.3 us
  Pallas kernels: 17.9 us -> 14.6 us
    all_to_all x0 -> x2, blocking collectives: none -> 18.3 us  [the longest x1 9.75 us: local(): sums = lax.all_to_all(sums, 'row', 0, 0, tiled=True)]
    ppermute x51 -> x44, starting transfers between devices: 54.7 us -> 46.7 us  [trade(): return lax.ppermute(part, axis, [(i, i ^ d) for i in range(n)])]
    ppermute x51 -> x44, waiting for transfers between devices: 29 us -> 22.3 us  [trade(): return lax.ppermute(part, axis, [(i, i ^ d) for i in range(n)])]
    pallas_call x13, Pallas kernels: 17.9 us -> 14.6 us  [call(): pl.pallas_call(lambda *refs: kernel(*refs[len(after):]), out_shape=out_sh...]
  transfers between devices with their start and end apart: 51 -> 44, of which waited for: 30 -> 24; matrix products, arithmetic and copies ran while one was open for 0% -> 0% of each run, Pallas kernels for 5% -> 5%
where the time goes in v11:
time: 106 us
  starting transfers between devices  46.7 us (44%)
  waiting for transfers between devices  22.3 us (21%)
  blocking collectives  18.3 us (17%)
  Pallas kernels  14.6 us (14%)
  local copies, waits for them, and re-layouts  2.89 us (3%)
    ppermute x44, starting transfers between devices, trade(): return lax.ppermute(part, axis, [(i, i ^ d) for i in range(n)])  46.7 us
    ppermute x44, waiting for transfers between devices, trade(): return lax.ppermute(part, axis, [(i, i ^ d) for i in range(n)])  22.3 us
    pallas_call x13, Pallas kernels, call(): pl.pallas_call(lambda *refs: kernel(*refs[len(after):]), out_shape=out_sh...  14.6 us
    all_to_all x1, blocking collectives, local(): sums = lax.all_to_all(sums, 'row', 0, 0, tiled=True)  9.75 us
    all_to_all x1, blocking collectives, local(): sums = jnp.sum(lax.all_to_all(sums, 'col', 0, 0, tiled=True), 0)  8.52 us
    unnamed x12, local copies, waits for them, and re-layouts  2.85 us
  transfers between devices with their start and end apart: 44, of which 24 were waited for; matrix products, arithmetic and copies ran while one was open for 0% of the time, Pallas kernels for 5%

profile of v11, /device:TPU:0, one launch (start us, length us, event | category | flops | bytes accessed | tf_op | source)
XLA Modules:
  0.0 105.7 jit_solution(15339982238929355726)
XLA Ops:
  0.7 0.7 copy-done.4
  1.4 0.9 copy-done.2
  2.3 0.6 shard_map.59
  2.9 4.1 %collective-permute-start.8 = (bf16[8,64,128]{2,1,0:T(8,128)(2,1)S(1)}, bf16[8,64,128]{2,1,0:T(8,128)(2,1)S(1)}, u32[]{:S(2)}, u32[]{:S(2)}) collective-permute-start(bf16[8,64,128]{2,1,0:T(8,128)(2,1)S(1)} %get-tuple-element.40.refs_2_.refs_3_), channel_id=1, source_target_pairs={{0,16},{8,24},{16,0},{24,8},{1,17},{9,25},{17,1},{25,9},{2,18},{10... | collective-permute-start | bytes 393224 | tf_op jit(solution)/shard_map/ppermute | solution.py:38
  7.0 1.6 %collective-permute-start.7 = (bf16[7,64,128]{2,1,0:T(8,128)(2,1)S(1)}, bf16[7,64,128]{2,1,0:T(8,128)(2,1)S(1)}, u32[]{:S(2)}, u32[]{:S(2)}) collective-permute-start(bf16[7,64,128]{2,1,0:T(8,128)(2,1)S(1)} %slice.18), channel_id=1, source_target_pairs={{0,8},{8,0},{16,24},{24,16},{1,9},{9,1},{17,25},{25,17},{2,10},{10... | collective-permute-start | bytes 344072 | tf_op jit(solution)/shard_map/ppermute | solution.py:38
  8.7 2.4 %collective-permute-start.2 = (bf16[8,64,128]{2,1,0:T(8,128)(2,1)S(1)}, bf16[8,64,128]{2,1,0:T(8,128)(2,1)S(1)}, u32[]{:S(2)}, u32[]{:S(2)}) collective-permute-start(bf16[8,64,128]{2,1,0:T(8,128)(2,1)S(1)} %get-tuple-element.40.refs_2_.refs_3_), channel_id=1, source_target_pairs={{0,6},{1,7},{2,4},{3,5},{4,2},{5,3},{6,0},{7,1},{8,14},{9,15},{10,... | collective-permute-start | bytes 393224 | tf_op jit(solution)/shard_map/ppermute | solution.py:38
  12.2 1.4 %collective-permute-done.7.refs_5_ = bf16[7,64,128]{2,1,0:T(8,128)(2,1)S(1)} collective-permute-done((bf16[7,64,128]{2,1,0:T(8,128)(2,1)S(1)}, bf16[7,64,128]{2,1,0:T(8,128)(2,1)S(1)}, u32[]{:S(2)}, u32[]{:S(2)}) %collective-permute-start.7) | collective-permute-done | bytes 114720 | tf_op jit(solution)/shard_map/ppermute | solution.py:38
  13.5 1.3 %collective-permute-start.9 = (bf16[9,64,128]{2,1,0:T(8,128)(2,1)S(1)}, bf16[9,64,128]{2,1,0:T(8,128)(2,1)S(1)}, u32[]{:S(2)}, u32[]{:S(2)}) collective-permute-start(bf16[9,64,128]{2,1,0:T(8,128)(2,1)S(1)} %pad_maximum_fusion), channel_id=1, source_target_pairs={{0,8},{8,0},{16,24},{24,16},{1,9},{9,1},{17,25},{25,17},{2,10},{10... | collective-permute-start | bytes 442376 | tf_op jit(solution)/shard_map/ppermute | solution.py:38
  15.3 1.7 %collective-permute-done.1.refs_4_ = bf16[8,64,128]{2,1,0:T(8,128)(2,1)S(1)} collective-permute-done((bf16[8,64,128]{2,1,0:T(8,128)(2,1)S(1)}, bf16[8,64,128]{2,1,0:T(8,128)(2,1)S(1)}, u32[]{:S(2)}, u32[]{:S(2)}) %collective-permute-start.1) | collective-permute-done | bytes 131104 | tf_op jit(solution)/shard_map/ppermute | solution.py:38
  17.6 1.2 %copy-done = bf16[1,1,32,128,128]{4,3,2,1,0:T(8,128)(2,1)S(1)} copy-done((bf16[1,1,32,128,128]{4,3,2,1,0:T(8,128)(2,1)S(1)}, bf16[1,1,32,128,128]{4,3,2,1,0:T(8,128)(2,1)}, u32[]{:S(2)}) %copy-start) | copy-done | bytes 1048600
  18.8 1.5 %shard_map.60 = (f32[64,128]{1,0:T(8,128)S(1)}, f32[32,128]{1,0:T(8,128)S(1)}) custom-call(s32[3,32]{1,0:T(4,128)S(1)} %get-tuple-element.39.refs_0_.refs_1_, bf16[32,128,128]{2,1,0:T(8,128)(2,1)S(1)} %bitcast.5), custom_call_target="tpu_custom_call" | custom-call | flops 33554432 | bytes 1048960 | tf_op jit(solution)/shard_map/pallas_call | solution.py:25
  20.4 1.1 %shard_map.61 = (f32[8,64,128]{2,1,0:T(8,128)S(1)}, bf16[528,128]{1,0:T(8,128)(2,1)S(1)}, bf16[528,128]{1,0:T(8,128)(2,1)S(1)}, bf16[528,128]{1,0:T(8,128)(2,1)S(1)}) custom-call(s32[3,32]{1,0:T(4,128)S(1)} %get-tuple-element.39.refs_0_.refs_1_, bf16[32,128,128]{2,1,0:T(8,128)(2,1)S(1)} %bitcast.6, ...), custom_call_target="tpu_custom_call" | custom-call | flops 67108864 | bytes 2113920 | tf_op jit(solution)/shard_map/pallas_call | solution.py:25
  21.5 1.5 %shard_map.62 = (f32[4,8,64,128]{3,2,1,0:T(8,128)S(1)}, bf16[4,528,128]{2,1,0:T(8,128)(2,1)S(1)}) custom-call(f32[8,64,128]{2,1,0:T(8,128)S(1)} %get-tuple-element.42.refs_0_.refs_4_, s32[3,32]{1,0:T(4,128)S(1)} %get-tuple-element.39.refs_0_.refs_1_, bf16[32,128,128]{2,1,0:T(8,128)(2,1)S(1)} %bitcast.7, ...), custom_call_target="tpu_custom_call" | custom-call | flops 67108864 | bytes 1606016 | tf_op jit(solution)/shard_map/pallas_call | solution.py:25
  23.6 1.3 %collective-permute-start.15 = (bf16[528,128]{1,0:T(8,128)(2,1)S(1)}, bf16[528,128]{1,0:T(8,128)(2,1)S(1)}, u32[]{:S(2)}, u32[]{:S(2)}) collective-permute-start(bf16[528,128]{1,0:T(8,128)(2,1)S(1)} %get-tuple-element.54), channel_id=1, source_target_pairs={{0,16},{8,24},{16,0},{24,8},{1,17},{9,25},{17,1},{25,9},{2,18},{10... | collective-permute-start | bytes 405512 | tf_op jit(solution)/shard_map/ppermute | solution.py:38
  24.9 2.6 %collective-permute-start.16 = (bf16[528,128]{1,0:T(8,128)(2,1)S(1)}, bf16[528,128]{1,0:T(8,128)(2,1)S(1)}, u32[]{:S(2)}, u32[]{:S(2)}) collective-permute-start(bf16[528,128]{1,0:T(8,128)(2,1)S(1)} %get-tuple-element.55), channel_id=1, source_target_pairs={{0,24},{8,16},{16,8},{24,0},{1,25},{9,17},{17,9},{25,1},{2,26},{10... | collective-permute-start | bytes 405512 | tf_op jit(solution)/shard_map/ppermute | solution.py:38
  27.7 1.6 %collective-permute-start.11 = (bf16[528,128]{1,0:T(8,128)(2,1)S(1)}, bf16[528,128]{1,0:T(8,128)(2,1)S(1)}, u32[]{:S(2)}, u32[]{:S(2)}) collective-permute-start(bf16[528,128]{1,0:T(8,128)(2,1)S(1)} %get-tuple-element.50), channel_id=1, source_target_pairs={{0,2},{1,3},{2,0},{3,1},{4,6},{5,7},{6,4},{7,5},{8,10},{9,11},{10,... | collective-permute-start | bytes 405512 | tf_op jit(solution)/shard_map/ppermute | solution.py:38
  29.3 0.8 collective-permute-start.12
  30.1 1.2 %collective-permute-done.14.refs_8_ = bf16[528,128]{1,0:T(8,128)(2,1)S(1)} collective-permute-done((bf16[528,128]{1,0:T(8,128)(2,1)S(1)}, bf16[528,128]{1,0:T(8,128)(2,1)S(1)}, u32[]{:S(2)}, u32[]{:S(2)}) %collective-permute-start.14) | collective-permute-done | bytes 135200 | tf_op jit(solution)/shard_map/ppermute | solution.py:38
  31.3 2.1 %collective-permute-start.13 = (bf16[528,128]{1,0:T(8,128)(2,1)S(1)}, bf16[528,128]{1,0:T(8,128)(2,1)S(1)}, u32[]{:S(2)}, u32[]{:S(2)}) collective-permute-start(bf16[528,128]{1,0:T(8,128)(2,1)S(1)} %get-tuple-element.52), channel_id=1, source_target_pairs={{0,6},{1,7},{2,4},{3,5},{4,2},{5,3},{6,0},{7,1},{8,14},{9,15},{10,... | collective-permute-start | bytes 405512 | tf_op jit(solution)/shard_map/ppermute | solution.py:38
  33.4 3.4 %collective-permute-done.15.refs_9_ = bf16[528,128]{1,0:T(8,128)(2,1)S(1)} collective-permute-done((bf16[528,128]{1,0:T(8,128)(2,1)S(1)}, bf16[528,128]{1,0:T(8,128)(2,1)S(1)}, u32[]{:S(2)}, u32[]{:S(2)}) %collective-permute-start.15) | collective-permute-done | bytes 135200 | tf_op jit(solution)/shard_map/ppermute | solution.py:38
  37.5 2.7 %collective-permute-start.25 = (bf16[8,64,128]{2,1,0:T(8,128)(2,1)S(1)}, bf16[8,64,128]{2,1,0:T(8,128)(2,1)S(1)}, u32[]{:S(2)}, u32[]{:S(2)}) collective-permute-start(bf16[8,64,128]{2,1,0:T(8,128)(2,1)S(1)} %get-tuple-element.58.refs_2_.refs_3_), channel_id=1, source_target_pairs={{0,16},{8,24},{16,0},{24,8},{1,17},{9,25},{17,1},{25,9},{2,18},{10... | collective-permute-start | bytes 393224 | tf_op jit(solution)/shard_map/ppermute | solution.py:38
  40.4 2.5 %collective-permute-start.19 = (bf16[8,64,128]{2,1,0:T(8,128)(2,1)S(1)}, bf16[8,64,128]{2,1,0:T(8,128)(2,1)S(1)}, u32[]{:S(2)}, u32[]{:S(2)}) collective-permute-start(bf16[8,64,128]{2,1,0:T(8,128)(2,1)S(1)} %get-tuple-element.58.refs_2_.refs_3_), channel_id=1, source_target_pairs={{0,6},{1,7},{2,4},{3,5},{4,2},{5,3},{6,0},{7,1},{8,14},{9,15},{10,... | collective-permute-start | bytes 393224 | tf_op jit(solution)/shard_map/ppermute | solution.py:38
  42.8 0.5 collective-permute-start.18
  43.9 2.0 %collective-permute-done.24.refs_5_ = bf16[7,64,128]{2,1,0:T(8,128)(2,1)S(1)} collective-permute-done((bf16[7,64,128]{2,1,0:T(8,128)(2,1)S(1)}, bf16[7,64,128]{2,1,0:T(8,128)(2,1)S(1)}, u32[]{:S(2)}, u32[]{:S(2)}) %collective-permute-start.24) | collective-permute-done | bytes 114720 | tf_op jit(solution)/shard_map/ppermute | solution.py:38
  46.2 1.4 %collective-permute-start.26 = (bf16[9,64,128]{2,1,0:T(8,128)(2,1)S(1)}, bf16[9,64,128]{2,1,0:T(8,128)(2,1)S(1)}, u32[]{:S(2)}, u32[]{:S(2)}) collective-permute-start(bf16[9,64,128]{2,1,0:T(8,128)(2,1)S(1)} %pad_maximum_fusion.1), channel_id=1, source_target_pairs={{0,8},{8,0},{16,24},{24,16},{1,9},{9,1},{17,25},{25,17},{2,10},{10... | collective-permute-start | bytes 442376 | tf_op jit(solution)/shard_map/ppermute | solution.py:38
  49.1 0.8 collective-permute-done.22.refs_8_
  50.1 1.1 %shard_map.65 = (f32[8,64,128]{2,1,0:T(8,128)S(1)}, bf16[512,128]{1,0:T(8,128)(2,1)S(1)}, bf16[512,128]{1,0:T(8,128)(2,1)S(1)}, bf16[512,128]{1,0:T(8,128)(2,1)S(1)}) custom-call(s32[3,32]{1,0:T(4,128)S(1)} %get-tuple-element.39.refs_0_.refs_1_, bf16[32,128,128]{2,1,0:T(8,128)(2,1)S(1)} %bitcast.8, ...), custom_call_target="tpu_custom_call" | custom-call | flops 67108864 | bytes 2097536 | tf_op jit(solution)/shard_map/pallas_call | solution.py:25
  51.5 1.5 %shard_map.66 = (f32[4,8,64,128]{3,2,1,0:T(8,128)S(1)}, bf16[4,512,128]{2,1,0:T(8,128)(2,1)S(1)}) custom-call(f32[8,64,128]{2,1,0:T(8,128)S(1)} %get-tuple-element.59.refs_0_.refs_4_, s32[3,32]{1,0:T(4,128)S(1)} %get-tuple-element.39.refs_0_.refs_1_, bf16[32,128,128]{2,1,0:T(8,128)(2,1)S(1)} %bitcast.9, ...), custom_call_target="tpu_custom_call" | custom-call | flops 67108864 | bytes 1573248 | tf_op jit(solution)/shard_map/pallas_call | solution.py:25
  53.2 1.7 %collective-permute-start.31 = (bf16[512,128]{1,0:T(8,128)(2,1)S(1)}, bf16[512,128]{1,0:T(8,128)(2,1)S(1)}, u32[]{:S(2)}, u32[]{:S(2)}) collective-permute-start(bf16[512,128]{1,0:T(8,128)(2,1)S(1)} %get-tuple-element.68), channel_id=1, source_target_pairs={{0,8},{8,0},{16,24},{24,16},{1,9},{9,1},{17,25},{25,17},{2,10},{10... | collective-permute-start | bytes 393224 | tf_op jit(solution)/shard_map/ppermute | solution.py:38
  54.9 0.7 collective-permute-start.32
  55.6 2.0 %collective-permute-start.33 = (bf16[512,128]{1,0:T(8,128)(2,1)S(1)}, bf16[512,128]{1,0:T(8,128)(2,1)S(1)}, u32[]{:S(2)}, u32[]{:S(2)}) collective-permute-start(bf16[512,128]{1,0:T(8,128)(2,1)S(1)} %get-tuple-element.70), channel_id=1, source_target_pairs={{0,24},{8,16},{16,8},{24,0},{1,25},{9,17},{17,9},{25,1},{2,26},{10... | collective-permute-start | bytes 393224 | tf_op jit(solution)/shard_map/ppermute | solution.py:38
  57.7 1.6 %collective-permute-start.28 = (bf16[512,128]{1,0:T(8,128)(2,1)S(1)}, bf16[512,128]{1,0:T(8,128)(2,1)S(1)}, u32[]{:S(2)}, u32[]{:S(2)}) collective-permute-start(bf16[512,128]{1,0:T(8,128)(2,1)S(1)} %get-tuple-element.65), channel_id=1, source_target_pairs={{0,2},{1,3},{2,0},{3,1},{4,6},{5,7},{6,4},{7,5},{8,10},{9,11},{10,... | collective-permute-start | bytes 393224 | tf_op jit(solution)/shard_map/ppermute | solution.py:38
  59.3 1.5 %collective-permute-start.29 = (bf16[512,128]{1,0:T(8,128)(2,1)S(1)}, bf16[512,128]{1,0:T(8,128)(2,1)S(1)}, u32[]{:S(2)}, u32[]{:S(2)}) collective-permute-start(bf16[512,128]{1,0:T(8,128)(2,1)S(1)} %get-tuple-element.66), channel_id=1, source_target_pairs={{0,4},{1,5},{2,6},{3,7},{4,0},{5,1},{6,2},{7,3},{8,12},{9,13},{10,... | collective-permute-start | bytes 393224 | tf_op jit(solution)/shard_map/ppermute | solution.py:38
  60.8 2.3 %collective-permute-start.30 = (bf16[512,128]{1,0:T(8,128)(2,1)S(1)}, bf16[512,128]{1,0:T(8,128)(2,1)S(1)}, u32[]{:S(2)}, u32[]{:S(2)}) collective-permute-start(bf16[512,128]{1,0:T(8,128)(2,1)S(1)} %get-tuple-element.67), channel_id=1, source_target_pairs={{0,6},{1,7},{2,4},{3,5},{4,2},{5,3},{6,0},{7,1},{8,14},{9,15},{10,... | collective-permute-start | bytes 393224 | tf_op jit(solution)/shard_map/ppermute | solution.py:38
  63.1 4.7 %collective-permute-done.32.refs_9_ = bf16[512,128]{1,0:T(8,128)(2,1)S(1)} collective-permute-done((bf16[512,128]{1,0:T(8,128)(2,1)S(1)}, bf16[512,128]{1,0:T(8,128)(2,1)S(1)}, u32[]{:S(2)}, u32[]{:S(2)}) %collective-permute-start.32) | collective-permute-done | bytes 131104 | tf_op jit(solution)/shard_map/ppermute | solution.py:38
  67.8 0.8 shard_map.68
  68.6 2.7 %collective-permute-start.42 = (bf16[8,64,128]{2,1,0:T(8,128)(2,1)S(1)}, bf16[8,64,128]{2,1,0:T(8,128)(2,1)S(1)}, u32[]{:S(2)}, u32[]{:S(2)}) collective-permute-start(bf16[8,64,128]{2,1,0:T(8,128)(2,1)S(1)} %get-tuple-element.72.refs_2_.refs_3_), channel_id=1, source_target_pairs={{0,16},{8,24},{16,0},{24,8},{1,17},{9,25},{17,1},{25,9},{2,18},{10... | collective-permute-start | bytes 393224 | tf_op jit(solution)/shard_map/ppermute | solution.py:38
  71.4 1.8 %collective-permute-start.36 = (bf16[8,64,128]{2,1,0:T(8,128)(2,1)S(1)}, bf16[8,64,128]{2,1,0:T(8,128)(2,1)S(1)}, u32[]{:S(2)}, u32[]{:S(2)}) collective-permute-start(bf16[8,64,128]{2,1,0:T(8,128)(2,1)S(1)} %get-tuple-element.72.refs_2_.refs_3_), channel_id=1, source_target_pairs={{0,6},{1,7},{2,4},{3,5},{4,2},{5,3},{6,0},{7,1},{8,14},{9,15},{10,... | collective-permute-start | bytes 393224 | tf_op jit(solution)/shard_map/ppermute | solution.py:38
  73.2 1.2 %collective-permute-start.35 = (bf16[8,64,128]{2,1,0:T(8,128)(2,1)S(1)}, bf16[8,64,128]{2,1,0:T(8,128)(2,1)S(1)}, u32[]{:S(2)}, u32[]{:S(2)}) collective-permute-start(bf16[8,64,128]{2,1,0:T(8,128)(2,1)S(1)} %get-tuple-element.72.refs_2_.refs_3_), channel_id=1, source_target_pairs={{0,4},{1,5},{2,6},{3,7},{4,0},{5,1},{6,2},{7,3},{8,12},{9,13},{10,... | collective-permute-start | bytes 393224 | tf_op jit(solution)/shard_map/ppermute | solution.py:38
  74.4 0.5 collective-permute-start.34
  75.0 2.0 %collective-permute-done.41.refs_5_ = bf16[7,64,128]{2,1,0:T(8,128)(2,1)S(1)} collective-permute-done((bf16[7,64,128]{2,1,0:T(8,128)(2,1)S(1)}, bf16[7,64,128]{2,1,0:T(8,128)(2,1)S(1)}, u32[]{:S(2)}, u32[]{:S(2)}) %collective-permute-start.41) | collective-permute-done | bytes 114720 | tf_op jit(solution)/shard_map/ppermute | solution.py:38
  77.2 1.1 %collective-permute-start.43 = (bf16[9,64,128]{2,1,0:T(8,128)(2,1)S(1)}, bf16[9,64,128]{2,1,0:T(8,128)(2,1)S(1)}, u32[]{:S(2)}, u32[]{:S(2)}) collective-permute-start(bf16[9,64,128]{2,1,0:T(8,128)(2,1)S(1)} %pad_maximum_fusion.2), channel_id=1, source_target_pairs={{0,8},{8,0},{16,24},{24,16},{1,9},{9,1},{17,25},{25,17},{2,10},{10... | collective-permute-start | bytes 442376 | tf_op jit(solution)/shard_map/ppermute | solution.py:38
  80.1 0.6 collective-permute-done.39.refs_8_
  80.9 1.0 shard_map.69.refs_1_
  82.4 1.2 %shard_map.70 = f32[8,40,128]{2,1,0:T(8,128)S(1)} custom-call(s32[3,32]{1,0:T(4,128)S(1)} %get-tuple-element.39.refs_0_.refs_1_, bf16[64,4096]{1,0:T(8,128)(2,1)S(1)} %shard_map.69.refs_1_, f32[64,128]{1,0:T(8,128)S(1)} %get-tuple-element.73.refs_2_, bf16[8,64,128]{2,1,0:T(8,128)(2,1)S(1)} %get-tuple-element.72.refs_2_.refs_3_, ...), custom_call_target="tpu_custom_call" | custom-call | flops 33554432 | bytes 1081728 | tf_op jit(solution)/shard_map/pallas_call | solution.py:25
  83.7 8.5 %all_to_all.10 = f32[8,40,128]{2,1,0:T(8,128)S(1)} all-to-all(f32[8,40,128]{2,1,0:T(8,128)S(1)} %shard_map.70), channel_id=1, replica_groups=mesh['row'=4,'col'=8] {'col'}, dimensions={0} | all-to-all | bytes 327680 | tf_op jit(solution)/shard_map/all_to_all | solution.py:451
  92.2 9.8 %all_to_all.11.refs_1_ = f32[4,40,128]{2,1,0:T(8,128)S(1)} all-to-all(f32[4,40,128]{2,1,0:T(8,128)S(1)} %broadcast_in_dim.3), channel_id=1, replica_groups=mesh['row'=4,'col'=8] {'row'}, dimensions={0} | all-to-all | bytes 163840 | tf_op jit(solution)/shard_map/all_to_all | solution.py:453
  102.0 3.8 %shard_map.71 = (f32[64,1024]{1,0:T(8,128)}, f32[64,64]{1,0:T(8,128)}) custom-call(f32[64,1024]{1,0:T(8,128)S(1)} %get-tuple-element.71.refs_0_, f32[4,40,128]{2,1,0:T(8,128)S(1)} %all_to_all.11.refs_1_), custom_call_target="tpu_custom_call" | custom-call | bytes 344064 | tf_op jit(solution)/shard_map/pallas_call | solution.py:25
  (79 shorter events, 9.6 us)
Async XLA Ops:
  1.4 0.9 copy-start.2
  2.9 10.6 %collective-permute-start.8 = (bf16[8,64,128]{2,1,0:T(8,128)(2,1)S(1)}, bf16[8,64,128]{2,1,0:T(8,128)(2,1)S(1)}, u32[]{:S(2)}, u32[]{:S(2)}) collective-permute-start(bf16[8,64,128]{2,1,0:T(8,128)(2,1)S(1)} %get-tuple-element.40.refs_2_.refs_3_), channel_id=1, source_target_pairs={{0,16},{8,24},{16,0},{24,8},{1,17},{9,25},{17,1},{25,9},{2,18},{10... | collective-permute-start | bytes 393224 | tf_op jit(solution)/shard_map/ppermute | solution.py:38
  7.0 6.5 %collective-permute-start.7 = (bf16[7,64,128]{2,1,0:T(8,128)(2,1)S(1)}, bf16[7,64,128]{2,1,0:T(8,128)(2,1)S(1)}, u32[]{:S(2)}, u32[]{:S(2)}) collective-permute-start(bf16[7,64,128]{2,1,0:T(8,128)(2,1)S(1)} %slice.18), channel_id=1, source_target_pairs={{0,8},{8,0},{16,24},{24,16},{1,9},{9,1},{17,25},{25,17},{2,10},{10... | collective-permute-start | bytes 344072 | tf_op jit(solution)/shard_map/ppermute | solution.py:38
  8.7 6.6 %collective-permute-start.2 = (bf16[8,64,128]{2,1,0:T(8,128)(2,1)S(1)}, bf16[8,64,128]{2,1,0:T(8,128)(2,1)S(1)}, u32[]{:S(2)}, u32[]{:S(2)}) collective-permute-start(bf16[8,64,128]{2,1,0:T(8,128)(2,1)S(1)} %get-tuple-element.40.refs_2_.refs_3_), channel_id=1, source_target_pairs={{0,6},{1,7},{2,4},{3,5},{4,2},{5,3},{6,0},{7,1},{8,14},{9,15},{10,... | collective-permute-start | bytes 393224 | tf_op jit(solution)/shard_map/ppermute | solution.py:38
  11.1 5.9 %collective-permute-start.1 = (bf16[8,64,128]{2,1,0:T(8,128)(2,1)S(1)}, bf16[8,64,128]{2,1,0:T(8,128)(2,1)S(1)}, u32[]{:S(2)}, u32[]{:S(2)}) collective-permute-start(bf16[8,64,128]{2,1,0:T(8,128)(2,1)S(1)} %get-tuple-element.40.refs_2_.refs_3_), channel_id=1, source_target_pairs={{0,4},{1,5},{2,6},{3,7},{4,0},{5,1},{6,2},{7,3},{8,12},{9,13},{10,... | collective-permute-start | bytes 393224 | tf_op jit(solution)/shard_map/ppermute | solution.py:38
  11.6 5.5 %collective-permute-start = (bf16[8,64,128]{2,1,0:T(8,128)(2,1)S(1)}, bf16[8,64,128]{2,1,0:T(8,128)(2,1)S(1)}, u32[]{:S(2)}, u32[]{:S(2)}) collective-permute-start(bf16[8,64,128]{2,1,0:T(8,128)(2,1)S(1)} %get-tuple-element.40.refs_2_.refs_3_), channel_id=1, source_target_pairs={{0,2},{1,3},{2,0},{3,1},{4,6},{5,7},{6,4},{7,5},{8,10},{9,11},{10,... | collective-permute-start | bytes 393224 | tf_op jit(solution)/shard_map/ppermute | solution.py:38
  13.5 8.0 %collective-permute-start.9 = (bf16[9,64,128]{2,1,0:T(8,128)(2,1)S(1)}, bf16[9,64,128]{2,1,0:T(8,128)(2,1)S(1)}, u32[]{:S(2)}, u32[]{:S(2)}) collective-permute-start(bf16[9,64,128]{2,1,0:T(8,128)(2,1)S(1)} %pad_maximum_fusion), channel_id=1, source_target_pairs={{0,8},{8,0},{16,24},{24,16},{1,9},{9,1},{17,25},{25,17},{2,10},{10... | collective-permute-start | bytes 442376 | tf_op jit(solution)/shard_map/ppermute | solution.py:38
  14.8 5.5 %collective-permute-start.3 = (bf16[8,64,128]{2,1,0:T(8,128)(2,1)S(1)}, bf16[8,64,128]{2,1,0:T(8,128)(2,1)S(1)}, u32[]{:S(2)}, u32[]{:S(2)}) collective-permute-start(bf16[8,64,128]{2,1,0:T(8,128)(2,1)S(1)} %get-tuple-element.40.refs_2_.refs_3_), channel_id=1, source_target_pairs={{0,1},{1,0},{2,3},{3,2},{4,5},{5,4},{6,7},{7,6},{8,9},{9,8},{10,11... | collective-permute-start | bytes 393224 | tf_op jit(solution)/shard_map/ppermute | solution.py:38
  15.2 5.1 %collective-permute-start.6 = (bf16[8,64,128]{2,1,0:T(8,128)(2,1)S(1)}, bf16[8,64,128]{2,1,0:T(8,128)(2,1)S(1)}, u32[]{:S(2)}, u32[]{:S(2)}) collective-permute-start(bf16[8,64,128]{2,1,0:T(8,128)(2,1)S(1)} %collective-permute-done.2.refs_5_), channel_id=1, source_target_pairs={{0,1},{1,0},{2,3},{3,2},{4,5},{5,4},{6,7},{7,6},{8,9},{9,8},{10,11... | collective-permute-start | bytes 393224 | tf_op jit(solution)/shard_map/ppermute | solution.py:38
  17.0 3.3 %collective-permute-start.5 = (bf16[8,64,128]{2,1,0:T(8,128)(2,1)S(1)}, bf16[8,64,128]{2,1,0:T(8,128)(2,1)S(1)}, u32[]{:S(2)}, u32[]{:S(2)}) collective-permute-start(bf16[8,64,128]{2,1,0:T(8,128)(2,1)S(1)} %collective-permute-done.1.refs_4_), channel_id=1, source_target_pairs={{0,1},{1,0},{2,3},{3,2},{4,5},{5,4},{6,7},{7,6},{8,9},{9,8},{10,11... | collective-permute-start | bytes 393224 | tf_op jit(solution)/shard_map/ppermute | solution.py:38
  17.1 3.2 %collective-permute-start.4 = (bf16[8,64,128]{2,1,0:T(8,128)(2,1)S(1)}, bf16[8,64,128]{2,1,0:T(8,128)(2,1)S(1)}, u32[]{:S(2)}, u32[]{:S(2)}) collective-permute-start(bf16[8,64,128]{2,1,0:T(8,128)(2,1)S(1)} %collective-permute-done.refs_3_), channel_id=1, source_target_pairs={{0,1},{1,0},{2,3},{3,2},{4,5},{5,4},{6,7},{7,6},{8,9},{9,8},{10,11... | collective-permute-start | bytes 393224 | tf_op jit(solution)/shard_map/ppermute | solution.py:38
  17.6 1.2 %copy-start = (bf16[1,1,32,128,128]{4,3,2,1,0:T(8,128)(2,1)S(1)}, bf16[1,1,32,128,128]{4,3,2,1,0:T(8,128)(2,1)}, u32[]{:S(2)}) copy-start(bf16[1,1,32,128,128]{4,3,2,1,0:T(8,128)(2,1)} %param.4) | copy-start | bytes 3145732
  18.8 1.6 %copy-start.1 = (bf16[1,1,32,128,128]{4,3,2,1,0:T(8,128)(2,1)S(1)}, bf16[1,1,32,128,128]{4,3,2,1,0:T(8,128)(2,1)}, u32[]{:S(2)}) copy-start(bf16[1,1,32,128,128]{4,3,2,1,0:T(8,128)(2,1)} %param.4) | copy-start | bytes 3145732
  23.0 4.5 %collective-permute-start.10 = (bf16[4,528,128]{2,1,0:T(8,128)(2,1)S(1)}, bf16[4,528,128]{2,1,0:T(8,128)(2,1)S(1)}, u32[]{:S(2)}, u32[]{:S(2)}) collective-permute-start(bf16[4,528,128]{2,1,0:T(8,128)(2,1)S(1)} %get-tuple-element.47), channel_id=1, source_target_pairs={{0,1},{1,0},{2,3},{3,2},{4,5},{5,4},{6,7},{7,6},{8,9},{9,8},{10,11... | collective-permute-start | bytes 1622024 | tf_op jit(solution)/shard_map/ppermute | solution.py:38
  23.2 8.1 %collective-permute-start.14 = (bf16[528,128]{1,0:T(8,128)(2,1)S(1)}, bf16[528,128]{1,0:T(8,128)(2,1)S(1)}, u32[]{:S(2)}, u32[]{:S(2)}) collective-permute-start(bf16[528,128]{1,0:T(8,128)(2,1)S(1)} %get-tuple-element.53), channel_id=1, source_target_pairs={{0,8},{8,0},{16,24},{24,16},{1,9},{9,1},{17,25},{25,17},{2,10},{10... | collective-permute-start | bytes 405512 | tf_op jit(solution)/shard_map/ppermute | solution.py:38
  23.6 13.2 %collective-permute-start.15 = (bf16[528,128]{1,0:T(8,128)(2,1)S(1)}, bf16[528,128]{1,0:T(8,128)(2,1)S(1)}, u32[]{:S(2)}, u32[]{:S(2)}) collective-permute-start(bf16[528,128]{1,0:T(8,128)(2,1)S(1)} %get-tuple-element.54), channel_id=1, source_target_pairs={{0,16},{8,24},{16,0},{24,8},{1,17},{9,25},{17,1},{25,9},{2,18},{10... | collective-permute-start | bytes 405512 | tf_op jit(solution)/shard_map/ppermute | solution.py:38
  24.9 11.9 %collective-permute-start.16 = (bf16[528,128]{1,0:T(8,128)(2,1)S(1)}, bf16[528,128]{1,0:T(8,128)(2,1)S(1)}, u32[]{:S(2)}, u32[]{:S(2)}) collective-permute-start(bf16[528,128]{1,0:T(8,128)(2,1)S(1)} %get-tuple-element.55), channel_id=1, source_target_pairs={{0,24},{8,16},{16,8},{24,0},{1,25},{9,17},{17,9},{25,1},{2,26},{10... | collective-permute-start | bytes 405512 | tf_op jit(solution)/shard_map/ppermute | solution.py:38
  27.6 9.8 %copy-start.3 = (f32[64,1024]{1,0:T(8,128)S(1)}, f32[64,1024]{1,0:T(8,128)}, u32[]{:S(2)}) copy-start(f32[64,1024]{1,0:T(8,128)} %refs_0_.3) | copy-start | bytes 786436
  27.7 9.1 %collective-permute-start.11 = (bf16[528,128]{1,0:T(8,128)(2,1)S(1)}, bf16[528,128]{1,0:T(8,128)(2,1)S(1)}, u32[]{:S(2)}, u32[]{:S(2)}) collective-permute-start(bf16[528,128]{1,0:T(8,128)(2,1)S(1)} %get-tuple-element.50), channel_id=1, source_target_pairs={{0,2},{1,3},{2,0},{3,1},{4,6},{5,7},{6,4},{7,5},{8,10},{9,11},{10,... | collective-permute-start | bytes 405512 | tf_op jit(solution)/shard_map/ppermute | solution.py:38
  29.3 7.5 %collective-permute-start.12 = (bf16[528,128]{1,0:T(8,128)(2,1)S(1)}, bf16[528,128]{1,0:T(8,128)(2,1)S(1)}, u32[]{:S(2)}, u32[]{:S(2)}) collective-permute-start(bf16[528,128]{1,0:T(8,128)(2,1)S(1)} %get-tuple-element.51), channel_id=1, source_target_pairs={{0,4},{1,5},{2,6},{3,7},{4,0},{5,1},{6,2},{7,3},{8,12},{9,13},{10,... | collective-permute-start | bytes 405512 | tf_op jit(solution)/shard_map/ppermute | solution.py:38
  31.3 6.0 %collective-permute-start.13 = (bf16[528,128]{1,0:T(8,128)(2,1)S(1)}, bf16[528,128]{1,0:T(8,128)(2,1)S(1)}, u32[]{:S(2)}, u32[]{:S(2)}) collective-permute-start(bf16[528,128]{1,0:T(8,128)(2,1)S(1)} %get-tuple-element.52), channel_id=1, source_target_pairs={{0,6},{1,7},{2,4},{3,5},{4,2},{5,3},{6,0},{7,1},{8,14},{9,15},{10,... | collective-permute-start | bytes 405512 | tf_op jit(solution)/shard_map/ppermute | solution.py:38
  37.5 8.7 %collective-permute-start.25 = (bf16[8,64,128]{2,1,0:T(8,128)(2,1)S(1)}, bf16[8,64,128]{2,1,0:T(8,128)(2,1)S(1)}, u32[]{:S(2)}, u32[]{:S(2)}) collective-permute-start(bf16[8,64,128]{2,1,0:T(8,128)(2,1)S(1)} %get-tuple-element.58.refs_2_.refs_3_), channel_id=1, source_target_pairs={{0,16},{8,24},{16,0},{24,8},{1,17},{9,25},{17,1},{25,9},{2,18},{10... | collective-permute-start | bytes 393224 | tf_op jit(solution)/shard_map/ppermute | solution.py:38
  40.3 5.7 %collective-permute-start.24 = (bf16[7,64,128]{2,1,0:T(8,128)(2,1)S(1)}, bf16[7,64,128]{2,1,0:T(8,128)(2,1)S(1)}, u32[]{:S(2)}, u32[]{:S(2)}) collective-permute-start(bf16[7,64,128]{2,1,0:T(8,128)(2,1)S(1)} %slice.20), channel_id=1, source_target_pairs={{0,8},{8,0},{16,24},{24,16},{1,9},{9,1},{17,25},{25,17},{2,10},{10... | collective-permute-start | bytes 344072 | tf_op jit(solution)/shard_map/ppermute | solution.py:38
  40.4 7.2 %collective-permute-start.19 = (bf16[8,64,128]{2,1,0:T(8,128)(2,1)S(1)}, bf16[8,64,128]{2,1,0:T(8,128)(2,1)S(1)}, u32[]{:S(2)}, u32[]{:S(2)}) collective-permute-start(bf16[8,64,128]{2,1,0:T(8,128)(2,1)S(1)} %get-tuple-element.58.refs_2_.refs_3_), channel_id=1, source_target_pairs={{0,6},{1,7},{2,4},{3,5},{4,2},{5,3},{6,0},{7,1},{8,14},{9,15},{10,... | collective-permute-start | bytes 393224 | tf_op jit(solution)/shard_map/ppermute | solution.py:38
  42.8 5.8 %collective-permute-start.18 = (bf16[8,64,128]{2,1,0:T(8,128)(2,1)S(1)}, bf16[8,64,128]{2,1,0:T(8,128)(2,1)S(1)}, u32[]{:S(2)}, u32[]{:S(2)}) collective-permute-start(bf16[8,64,128]{2,1,0:T(8,128)(2,1)S(1)} %get-tuple-element.58.refs_2_.refs_3_), channel_id=1, source_target_pairs={{0,4},{1,5},{2,6},{3,7},{4,0},{5,1},{6,2},{7,3},{8,12},{9,13},{10,... | collective-permute-start | bytes 393224 | tf_op jit(solution)/shard_map/ppermute | solution.py:38
  43.4 5.3 %collective-permute-start.17 = (bf16[8,64,128]{2,1,0:T(8,128)(2,1)S(1)}, bf16[8,64,128]{2,1,0:T(8,128)(2,1)S(1)}, u32[]{:S(2)}, u32[]{:S(2)}) collective-permute-start(bf16[8,64,128]{2,1,0:T(8,128)(2,1)S(1)} %get-tuple-element.58.refs_2_.refs_3_), channel_id=1, source_target_pairs={{0,2},{1,3},{2,0},{3,1},{4,6},{5,7},{6,4},{7,5},{8,10},{9,11},{10,... | collective-permute-start | bytes 393224 | tf_op jit(solution)/shard_map/ppermute | solution.py:38
  46.2 5.2 %collective-permute-start.26 = (bf16[9,64,128]{2,1,0:T(8,128)(2,1)S(1)}, bf16[9,64,128]{2,1,0:T(8,128)(2,1)S(1)}, u32[]{:S(2)}, u32[]{:S(2)}) collective-permute-start(bf16[9,64,128]{2,1,0:T(8,128)(2,1)S(1)} %pad_maximum_fusion.1), channel_id=1, source_target_pairs={{0,8},{8,0},{16,24},{24,16},{1,9},{9,1},{17,25},{25,17},{2,10},{10... | collective-permute-start | bytes 442376 | tf_op jit(solution)/shard_map/ppermute | solution.py:38
  47.6 1.5 %collective-permute-start.20 = (bf16[8,64,128]{2,1,0:T(8,128)(2,1)S(1)}, bf16[8,64,128]{2,1,0:T(8,128)(2,1)S(1)}, u32[]{:S(2)}, u32[]{:S(2)}) collective-permute-start(bf16[8,64,128]{2,1,0:T(8,128)(2,1)S(1)} %get-tuple-element.58.refs_2_.refs_3_), channel_id=1, source_target_pairs={{0,1},{1,0},{2,3},{3,2},{4,5},{5,4},{6,7},{7,6},{8,9},{9,8},{10,11... | collective-permute-start | bytes 393224 | tf_op jit(solution)/shard_map/ppermute | solution.py:38
  47.6 1.5 %collective-permute-start.23 = (bf16[8,64,128]{2,1,0:T(8,128)(2,1)S(1)}, bf16[8,64,128]{2,1,0:T(8,128)(2,1)S(1)}, u32[]{:S(2)}, u32[]{:S(2)}) collective-permute-start(bf16[8,64,128]{2,1,0:T(8,128)(2,1)S(1)} %collective-permute-done.19.refs_5_), channel_id=1, source_target_pairs={{0,1},{1,0},{2,3},{3,2},{4,5},{5,4},{6,7},{7,6},{8,9},{9,8},{10,11... | collective-permute-start | bytes 393224 | tf_op jit(solution)/shard_map/ppermute | solution.py:38
  48.6 1.3 %collective-permute-start.22 = (bf16[8,64,128]{2,1,0:T(8,128)(2,1)S(1)}, bf16[8,64,128]{2,1,0:T(8,128)(2,1)S(1)}, u32[]{:S(2)}, u32[]{:S(2)}) collective-permute-start(bf16[8,64,128]{2,1,0:T(8,128)(2,1)S(1)} %collective-permute-done.18.refs_4_), channel_id=1, source_target_pairs={{0,1},{1,0},{2,3},{3,2},{4,5},{5,4},{6,7},{7,6},{8,9},{9,8},{10,11... | collective-permute-start | bytes 393224 | tf_op jit(solution)/shard_map/ppermute | solution.py:38
  48.7 1.4 %collective-permute-start.21 = (bf16[8,64,128]{2,1,0:T(8,128)(2,1)S(1)}, bf16[8,64,128]{2,1,0:T(8,128)(2,1)S(1)}, u32[]{:S(2)}, u32[]{:S(2)}) collective-permute-start(bf16[8,64,128]{2,1,0:T(8,128)(2,1)S(1)} %collective-permute-done.17.refs_3_), channel_id=1, source_target_pairs={{0,1},{1,0},{2,3},{3,2},{4,5},{5,4},{6,7},{7,6},{8,9},{9,8},{10,11... | collective-permute-start | bytes 393224 | tf_op jit(solution)/shard_map/ppermute | solution.py:38
  53.0 4.6 %collective-permute-start.27 = (bf16[4,512,128]{2,1,0:T(8,128)(2,1)S(1)}, bf16[4,512,128]{2,1,0:T(8,128)(2,1)S(1)}, u32[]{:S(2)}, u32[]{:S(2)}) collective-permute-start(bf16[4,512,128]{2,1,0:T(8,128)(2,1)S(1)} %get-tuple-element.63), channel_id=1, source_target_pairs={{0,1},{1,0},{2,3},{3,2},{4,5},{5,4},{6,7},{7,6},{8,9},{9,8},{10,11... | collective-permute-start | bytes 1572872 | tf_op jit(solution)/shard_map/ppermute | solution.py:38
  53.2 7.6 %collective-permute-start.31 = (bf16[512,128]{1,0:T(8,128)(2,1)S(1)}, bf16[512,128]{1,0:T(8,128)(2,1)S(1)}, u32[]{:S(2)}, u32[]{:S(2)}) collective-permute-start(bf16[512,128]{1,0:T(8,128)(2,1)S(1)} %get-tuple-element.68), channel_id=1, source_target_pairs={{0,8},{8,0},{16,24},{24,16},{1,9},{9,1},{17,25},{25,17},{2,10},{10... | collective-permute-start | bytes 393224 | tf_op jit(solution)/shard_map/ppermute | solution.py:38
  54.9 12.9 %collective-permute-start.32 = (bf16[512,128]{1,0:T(8,128)(2,1)S(1)}, bf16[512,128]{1,0:T(8,128)(2,1)S(1)}, u32[]{:S(2)}, u32[]{:S(2)}) collective-permute-start(bf16[512,128]{1,0:T(8,128)(2,1)S(1)} %get-tuple-element.69), channel_id=1, source_target_pairs={{0,16},{8,24},{16,0},{24,8},{1,17},{9,25},{17,1},{25,9},{2,18},{10... | collective-permute-start | bytes 393224 | tf_op jit(solution)/shard_map/ppermute | solution.py:38
  55.6 12.2 %collective-permute-start.33 = (bf16[512,128]{1,0:T(8,128)(2,1)S(1)}, bf16[512,128]{1,0:T(8,128)(2,1)S(1)}, u32[]{:S(2)}, u32[]{:S(2)}) collective-permute-start(bf16[512,128]{1,0:T(8,128)(2,1)S(1)} %get-tuple-element.70), channel_id=1, source_target_pairs={{0,24},{8,16},{16,8},{24,0},{1,25},{9,17},{17,9},{25,1},{2,26},{10... | collective-permute-start | bytes 393224 | tf_op jit(solution)/shard_map/ppermute | solution.py:38
  57.7 10.1 %collective-permute-start.28 = (bf16[512,128]{1,0:T(8,128)(2,1)S(1)}, bf16[512,128]{1,0:T(8,128)(2,1)S(1)}, u32[]{:S(2)}, u32[]{:S(2)}) collective-permute-start(bf16[512,128]{1,0:T(8,128)(2,1)S(1)} %get-tuple-element.65), channel_id=1, source_target_pairs={{0,2},{1,3},{2,0},{3,1},{4,6},{5,7},{6,4},{7,5},{8,10},{9,11},{10,... | collective-permute-start | bytes 393224 | tf_op jit(solution)/shard_map/ppermute | solution.py:38
  59.3 8.5 %collective-permute-start.29 = (bf16[512,128]{1,0:T(8,128)(2,1)S(1)}, bf16[512,128]{1,0:T(8,128)(2,1)S(1)}, u32[]{:S(2)}, u32[]{:S(2)}) collective-permute-start(bf16[512,128]{1,0:T(8,128)(2,1)S(1)} %get-tuple-element.66), channel_id=1, source_target_pairs={{0,4},{1,5},{2,6},{3,7},{4,0},{5,1},{6,2},{7,3},{8,12},{9,13},{10,... | collective-permute-start | bytes 393224 | tf_op jit(solution)/shard_map/ppermute | solution.py:38
  60.8 7.0 %collective-permute-start.30 = (bf16[512,128]{1,0:T(8,128)(2,1)S(1)}, bf16[512,128]{1,0:T(8,128)(2,1)S(1)}, u32[]{:S(2)}, u32[]{:S(2)}) collective-permute-start(bf16[512,128]{1,0:T(8,128)(2,1)S(1)} %get-tuple-element.67), channel_id=1, source_target_pairs={{0,6},{1,7},{2,4},{3,5},{4,2},{5,3},{6,0},{7,1},{8,14},{9,15},{10,... | collective-permute-start | bytes 393224 | tf_op jit(solution)/shard_map/ppermute | solution.py:38
  68.6 8.6 %collective-permute-start.42 = (bf16[8,64,128]{2,1,0:T(8,128)(2,1)S(1)}, bf16[8,64,128]{2,1,0:T(8,128)(2,1)S(1)}, u32[]{:S(2)}, u32[]{:S(2)}) collective-permute-start(bf16[8,64,128]{2,1,0:T(8,128)(2,1)S(1)} %get-tuple-element.72.refs_2_.refs_3_), channel_id=1, source_target_pairs={{0,16},{8,24},{16,0},{24,8},{1,17},{9,25},{17,1},{25,9},{2,18},{10... | collective-permute-start | bytes 393224 | tf_op jit(solution)/shard_map/ppermute | solution.py:38
  71.3 5.6 %collective-permute-start.41 = (bf16[7,64,128]{2,1,0:T(8,128)(2,1)S(1)}, bf16[7,64,128]{2,1,0:T(8,128)(2,1)S(1)}, u32[]{:S(2)}, u32[]{:S(2)}) collective-permute-start(bf16[7,64,128]{2,1,0:T(8,128)(2,1)S(1)} %slice.22), channel_id=1, source_target_pairs={{0,8},{8,0},{16,24},{24,16},{1,9},{9,1},{17,25},{25,17},{2,10},{10... | collective-permute-start | bytes 344072 | tf_op jit(solution)/shard_map/ppermute | solution.py:38
  71.4 7.3 %collective-permute-start.36 = (bf16[8,64,128]{2,1,0:T(8,128)(2,1)S(1)}, bf16[8,64,128]{2,1,0:T(8,128)(2,1)S(1)}, u32[]{:S(2)}, u32[]{:S(2)}) collective-permute-start(bf16[8,64,128]{2,1,0:T(8,128)(2,1)S(1)} %get-tuple-element.72.refs_2_.refs_3_), channel_id=1, source_target_pairs={{0,6},{1,7},{2,4},{3,5},{4,2},{5,3},{6,0},{7,1},{8,14},{9,15},{10,... | collective-permute-start | bytes 393224 | tf_op jit(solution)/shard_map/ppermute | solution.py:38
  73.2 6.1 %collective-permute-start.35 = (bf16[8,64,128]{2,1,0:T(8,128)(2,1)S(1)}, bf16[8,64,128]{2,1,0:T(8,128)(2,1)S(1)}, u32[]{:S(2)}, u32[]{:S(2)}) collective-permute-start(bf16[8,64,128]{2,1,0:T(8,128)(2,1)S(1)} %get-tuple-element.72.refs_2_.refs_3_), channel_id=1, source_target_pairs={{0,4},{1,5},{2,6},{3,7},{4,0},{5,1},{6,2},{7,3},{8,12},{9,13},{10,... | collective-permute-start | bytes 393224 | tf_op jit(solution)/shard_map/ppermute | solution.py:38
  74.4 5.1 %collective-permute-start.34 = (bf16[8,64,128]{2,1,0:T(8,128)(2,1)S(1)}, bf16[8,64,128]{2,1,0:T(8,128)(2,1)S(1)}, u32[]{:S(2)}, u32[]{:S(2)}) collective-permute-start(bf16[8,64,128]{2,1,0:T(8,128)(2,1)S(1)} %get-tuple-element.72.refs_2_.refs_3_), channel_id=1, source_target_pairs={{0,2},{1,3},{2,0},{3,1},{4,6},{5,7},{6,4},{7,5},{8,10},{9,11},{10,... | collective-permute-start | bytes 393224 | tf_op jit(solution)/shard_map/ppermute | solution.py:38
  77.2 5.2 %collective-permute-start.43 = (bf16[9,64,128]{2,1,0:T(8,128)(2,1)S(1)}, bf16[9,64,128]{2,1,0:T(8,128)(2,1)S(1)}, u32[]{:S(2)}, u32[]{:S(2)}) collective-permute-start(bf16[9,64,128]{2,1,0:T(8,128)(2,1)S(1)} %pad_maximum_fusion.2), channel_id=1, source_target_pairs={{0,8},{8,0},{16,24},{24,16},{1,9},{9,1},{17,25},{25,17},{2,10},{10... | collective-permute-start | bytes 442376 | tf_op jit(solution)/shard_map/ppermute | solution.py:38
  78.3 1.6 %collective-permute-start.37 = (bf16[8,64,128]{2,1,0:T(8,128)(2,1)S(1)}, bf16[8,64,128]{2,1,0:T(8,128)(2,1)S(1)}, u32[]{:S(2)}, u32[]{:S(2)}) collective-permute-start(bf16[8,64,128]{2,1,0:T(8,128)(2,1)S(1)} %get-tuple-element.72.refs_2_.refs_3_), channel_id=1, source_target_pairs={{0,1},{1,0},{2,3},{3,2},{4,5},{5,4},{6,7},{7,6},{8,9},{9,8},{10,11... | collective-permute-start | bytes 393224 | tf_op jit(solution)/shard_map/ppermute | solution.py:38
  78.7 1.3 %collective-permute-start.40 = (bf16[8,64,128]{2,1,0:T(8,128)(2,1)S(1)}, bf16[8,64,128]{2,1,0:T(8,128)(2,1)S(1)}, u32[]{:S(2)}, u32[]{:S(2)}) collective-permute-start(bf16[8,64,128]{2,1,0:T(8,128)(2,1)S(1)} %collective-permute-done.36.refs_5_), channel_id=1, source_target_pairs={{0,1},{1,0},{2,3},{3,2},{4,5},{5,4},{6,7},{7,6},{8,9},{9,8},{10,11... | collective-permute-start | bytes 393224 | tf_op jit(solution)/shard_map/ppermute | solution.py:38
  79.4 1.3 %collective-permute-start.39 = (bf16[8,64,128]{2,1,0:T(8,128)(2,1)S(1)}, bf16[8,64,128]{2,1,0:T(8,128)(2,1)S(1)}, u32[]{:S(2)}, u32[]{:S(2)}) collective-permute-start(bf16[8,64,128]{2,1,0:T(8,128)(2,1)S(1)} %collective-permute-done.35.refs_4_), channel_id=1, source_target_pairs={{0,1},{1,0},{2,3},{3,2},{4,5},{5,4},{6,7},{7,6},{8,9},{9,8},{10,11... | collective-permute-start | bytes 393224 | tf_op jit(solution)/shard_map/ppermute | solution.py:38
  79.5 1.5 %collective-permute-start.38 = (bf16[8,64,128]{2,1,0:T(8,128)(2,1)S(1)}, bf16[8,64,128]{2,1,0:T(8,128)(2,1)S(1)}, u32[]{:S(2)}, u32[]{:S(2)}) collective-permute-start(bf16[8,64,128]{2,1,0:T(8,128)(2,1)S(1)} %collective-permute-done.34.refs_3_), channel_id=1, source_target_pairs={{0,1},{1,0},{2,3},{3,2},{4,5},{5,4},{6,7},{7,6},{8,9},{9,8},{10,11... | collective-permute-start | bytes 393224 | tf_op jit(solution)/shard_map/ppermute | solution.py:38
  (2 other events, 1.3 us)

commit v12 on v11

--- a/solution.py
+++ b/solution.py
@@ -20,13 +20,13 @@
 DEGREE_ROWS = 16
 
 
-def call(kernel, out_shape, scratch, limit, args, flops=0, smem=0, after=()):
+def call(kernel, out_shape, scratch, limit, args, flops=0, smem=0, after=(), outs=None):
     moved = sum(x.size * x.dtype.itemsize for x in args)
     return pl.pallas_call(
         lambda *refs: kernel(*refs[len(after) :]),
         out_shape=out_shape,
         in_specs=[ANY] * len(after) + [SMEM] * smem + [VMEM] * (len(args) - smem),
-        out_specs=jax.tree.map(lambda _: VMEM, out_shape),
+        out_specs=outs or jax.tree.map(lambda _: VMEM, out_shape),
         scratch_shapes=scratch,
         compiler_params=pltpu.CompilerParams(vmem_limit_bytes=limit * 2**20),
         cost_estimate=pl.CostEstimate(flops=flops, bytes_accessed=moved, transcendentals=0),
@@ -47,18 +47,9 @@
     return [ref[:, k * width : (k + 1) * width] for k in range(ref.shape[1] // width)]
 
 
-def round_kernel(meta, rows_ref, cols_ref, vec_ref, out_ref, table_ref):
-    group, _, width = out_ref.shape
-    for k, piece in enumerate(tiles_first(vec_ref, width)):
+def round_kernel(vec_ref, out_ref):
+    for k, piece in enumerate(tiles_first(vec_ref, out_ref.shape[2])):
         out_ref[k] = piece.astype(BF16)
-    rows, cols = rows_ref[...], cols_ref[...]
-    col_apart = lax.div(cols, group) ^ meta[0]
-    row_apart = lax.div(rows, group) ^ meta[1]
-    row_halves = lax.rem(row_apart, 2) * meta[2] + lax.div(row_apart, 2)
-    inside = lax.rem(rows, group)
-    table_ref[0:1, :] = col_apart * group + lax.rem(cols, group)
-    table_ref[1:2, :] = row_apart * group + inside
-    table_ref[2:3, :] = row_halves * group + inside
 
 
 def split_degree(sums):
@@ -79,11 +70,18 @@
             at += count
 
 
-def degree_kernel(table, tiles_ref, row_ref, col_ref):
+def degree_kernel(group, meta, tile_rows, tile_cols, tiles_ref, row_ref, col_ref, table):
     row_ref[...] = jnp.zeros_like(row_ref)
     col_ref[...] = jnp.zeros_like(col_ref)
     ones = jnp.ones((DEGREE_ROWS, tiles_ref.shape[2]), BF16)
     for t in range(tiles_ref.shape[0]):
+        row, col = tile_rows[t], tile_cols[t]
+        apart = lax.div(row, group) ^ meta[1]
+        halves = lax.rem(apart, 2) * meta[2] + lax.div(apart, 2)
+        inside = lax.rem(row, group)
+        table[0, t] = (lax.div(col, group) ^ meta[0]) * group + lax.rem(col, group)
+        table[1, t] = apart * group + inside
+        table[2, t] = halves * group + inside
         for ref, place, dims in ((row_ref, table[2, t], NT), (col_ref, table[0, t], NN)):
             sums = lax.dot_general(ones, tiles_ref[t], dims, preferred_element_type=F32)
             ref[pl.ds(place, 1), :] += sums[:1]
@@ -273,10 +271,9 @@
     packed = jnp.where(col >= row, gram_ref[:, :vectors_n], projected)
     diagonal = jnp.sum(jnp.where(row == col, projected, 0.0), 0, keepdims=True)
     half = vectors_n // 2
+    out_ref[:half] = jnp.concatenate([packed[:half], packed[half:]], 1)
     diagonal = jnp.broadcast_to(diagonal, (8, vectors_n))
-    for d in range(out_ref.shape[0]):
-        out_ref[d, :half] = jnp.concatenate([packed[:half], packed[half:]], 1)
-        out_ref[d, half:] = jnp.concatenate([diagonal, jnp.zeros_like(diagonal)], 1)
+    out_ref[half:] = jnp.concatenate([diagonal, jnp.zeros_like(diagonal)], 1)
 
 
 def square_index(n):
@@ -326,10 +323,11 @@
     return jnp.concatenate(bands, 0)[:, n:]
 
 
-def last_kernel(total_nodes, filtered_ref, sums_ref, ritz_ref, rayleigh_ref):
+def last_kernel(total_nodes, filtered_ref, *refs):
+    parts, (ritz_ref, rayleigh_ref) = refs[:-2], refs[-2:]
     n = filtered_ref.shape[0]
     half = n // 2
-    sums = jnp.sum(sums_ref[...], 0) * (1.0 / total_nodes)
+    sums = tree_sum([part[...] for part in parts]) * (1.0 / total_nodes)
     packed = jnp.concatenate([sums[:half, :n], sums[:half, n:]], 0)
     row, col = square_index(n)
     upper = jnp.where(col > row, packed, 0.0)
@@ -346,6 +344,12 @@
     rayleigh_ref[...] = dot(half_way, inverse, NT)
     turned = dot(inverse, half_way, NT)
     ritz_ref[...] = dot(turned, dot(inverse, filtered_ref[...], NN), NN)
+
+
+def tree_sum(parts):
+    while len(parts) > 1:
+        parts = [a + b for a, b in zip(parts[::2], parts[1::2])]
+    return parts[0]
 
 
 def local(tiles, tile_rows, tile_cols, start):
@@ -388,7 +392,7 @@
         return held, chips + [trade(chip, "col", 1) for chip in chips]
 
     def apply(rounded, degree=()):
-        kept, swap, col_own, col_send = products(tiles, table, *gather(rounded), runs, degree)
+        kept, swap, col_own, col_send = products(tiles, table, *gather(rounded, degree), runs, degree)
         col_got = exchange(col_send, "row")
         row_own, *row_send = merge(kept, trade(swap, "col", 1), degree)
         if degree:
@@ -397,23 +401,18 @@
         sums = [row_own, col_own, *row_got, *col_got]
         return [own_degree, degree[1], *sums] if degree else sums
 
+    rounded = call(round_kernel, rounded_shape, [], 16, [start])
     meta = jnp.stack([lax.axis_index("row"), lax.axis_index("col"), chips_n]).astype(jnp.int32)
-    rounded, table = call(
-        round_kernel,
-        [rounded_shape, jax.ShapeDtypeStruct((3, tiles.shape[0]), jnp.int32)],
+    *degree, table = call(
+        functools.partial(degree_kernel, group),
+        [jax.ShapeDtypeStruct((n * group, width), F32) for n in (cols_n, rows_n)]
+        + [jax.ShapeDtypeStruct((3, tiles.shape[0]), jnp.int32)],
         [],
         16,
-        [meta, tile_rows[None], tile_cols[None], start],
-        smem=1,
-    )
-    degree = call(
-        degree_kernel,
-        [jax.ShapeDtypeStruct((n * group, width), F32) for n in (cols_n, rows_n)],
-        [],
-        16,
-        [table, tiles],
+        [meta, tile_rows, tile_cols, tiles],
         4 * tiles.size * DEGREE_ROWS,
-        1,
+        3,
+        outs=[VMEM, VMEM, SMEM],
     )
     first, rounded, degree = call(
         functools.partial(first_kernel, chips_n),
@@ -441,22 +440,21 @@
     )
     sums = call(
         functools.partial(form_kernel, runs[0]),
-        jax.ShapeDtypeStruct((cols_n, vectors_n // 2 + 8, 2 * vectors_n), F32),
+        jax.ShapeDtypeStruct((vectors_n // 2 + 8, 2 * vectors_n), F32),
         [pltpu.VMEM((rows_n * group, vectors_n, width), BF16), pltpu.VMEM(spread, BF16)],
         24,
         [table, left, gram, *col_parts],
         2 * vectors_n * spread[0] * spread[1],
         1,
     )
-    sums = jnp.sum(lax.all_to_all(sums, "col", 0, 0, tiled=True), 0)
-    sums = jnp.broadcast_to(sums, (rows_n, *sums.shape))
-    sums = lax.all_to_all(sums, "row", 0, 0, tiled=True)
+    sums = sums + trade(sums, "col", 1)
+    sums = tree_sum([sums, *exchange([sums] * (chips_n - 1), "col", 2)])
     return call(
         functools.partial(last_kernel, total_nodes),
         [vector_shape, jax.ShapeDtypeStruct((vectors_n, vectors_n), F32)],
         [],
         24,
-        [filtered, sums],
+        [filtered, sums, *exchange([sums] * (rows_n - 1), "row")],
     )
 
 

time: 106 us -> 101 us (0.953)
  blocking collectives: 18.3 us -> 0 us
  starting transfers between devices: 46.7 us -> 57.6 us
  waiting for transfers between devices: 22.3 us -> 25.1 us
    all_to_all x2 -> x0, blocking collectives: 18.3 us -> none  [the longest x1 9.75 us: local(): sums = lax.all_to_all(sums, 'row', 0, 0, tiled=True)]
    ppermute x44 -> x51, starting transfers between devices: 46.7 us -> 57.6 us  [trade(): return lax.ppermute(part, axis, [(i, i ^ d) for i in range(n)])]
    ppermute x44 -> x51, waiting for transfers between devices: 22.3 us -> 25.1 us  [trade(): return lax.ppermute(part, axis, [(i, i ^ d) for i in range(n)])]
  transfers between devices with their start and end apart: 44 -> 51, of which waited for: 24 -> 28; matrix products, arithmetic and copies ran while one was open for 0% -> 0% of each run, Pallas kernels for 5% -> 5%
where the time goes in v12:
time: 101 us
  starting transfers between devices  57.6 us (57%)
  waiting for transfers between devices  25.1 us (25%)
  Pallas kernels  14.5 us (14%)
  local copies, waits for them, and re-layouts  2.88 us (3%)
    ppermute x51, starting transfers between devices, trade(): return lax.ppermute(part, axis, [(i, i ^ d) for i in range(n)])  57.6 us
    ppermute x51, waiting for transfers between devices, trade(): return lax.ppermute(part, axis, [(i, i ^ d) for i in range(n)])  25.1 us
    pallas_call x13, Pallas kernels, call(): pl.pallas_call(lambda *refs: kernel(*refs[len(after):]), out_shape=out_sh...  14.5 us
    unnamed x12, local copies, waits for them, and re-layouts  2.85 us
  transfers between devices with their start and end apart: 51, of which 28 were waited for; matrix products, arithmetic and copies ran while one was open for 0% of the time, Pallas kernels for 5%

profile of v12, /device:TPU:0, one launch (start us, length us, event | category | flops | bytes accessed | tf_op | source)
XLA Modules:
  0.0 101.1 jit_solution(6430988567977615289)
XLA Ops:
  0.6 0.9 copy-done.2
  1.6 4.1 %collective-permute-start.8 = (bf16[8,64,128]{2,1,0:T(8,128)(2,1)S(1)}, bf16[8,64,128]{2,1,0:T(8,128)(2,1)S(1)}, u32[]{:S(2)}, u32[]{:S(2)}) collective-permute-start(bf16[8,64,128]{2,1,0:T(8,128)(2,1)S(1)} %shard_map.60.refs_2_.refs_3_), channel_id=1, source_target_pairs={{0,16},{8,24},{16,0},{24,8},{1,17},{9,25},{17,1},{25,9},{2,18},{10... | collective-permute-start | bytes 393224 | tf_op jit(solution)/shard_map/ppermute | solution.py:38
  5.7 2.4 %collective-permute-start.2 = (bf16[8,64,128]{2,1,0:T(8,128)(2,1)S(1)}, bf16[8,64,128]{2,1,0:T(8,128)(2,1)S(1)}, u32[]{:S(2)}, u32[]{:S(2)}) collective-permute-start(bf16[8,64,128]{2,1,0:T(8,128)(2,1)S(1)} %shard_map.60.refs_2_.refs_3_), channel_id=1, source_target_pairs={{0,6},{1,7},{2,4},{3,5},{4,2},{5,3},{6,0},{7,1},{8,14},{9,15},{10,... | collective-permute-start | bytes 393224 | tf_op jit(solution)/shard_map/ppermute | solution.py:38
  9.2 1.6 %collective-permute-start.7 = (bf16[7,64,128]{2,1,0:T(8,128)(2,1)S(1)}, bf16[7,64,128]{2,1,0:T(8,128)(2,1)S(1)}, u32[]{:S(2)}, u32[]{:S(2)}) collective-permute-start(bf16[7,64,128]{2,1,0:T(8,128)(2,1)S(1)} %slice.24), channel_id=1, source_target_pairs={{0,8},{8,0},{16,24},{24,16},{1,9},{9,1},{17,25},{25,17},{2,10},{10... | collective-permute-start | bytes 344072 | tf_op jit(solution)/shard_map/ppermute | solution.py:38
  11.6 1.2 %copy-done = bf16[1,1,32,128,128]{4,3,2,1,0:T(8,128)(2,1)S(1)} copy-done((bf16[1,1,32,128,128]{4,3,2,1,0:T(8,128)(2,1)S(1)}, bf16[1,1,32,128,128]{4,3,2,1,0:T(8,128)(2,1)}, u32[]{:S(2)}) %copy-start) | copy-done | bytes 1048600
  12.8 2.0 %shard_map.59 = (f32[64,128]{1,0:T(8,128)S(1)}, f32[32,128]{1,0:T(8,128)S(1)}, s32[3,32]{1,0:T(4,128)S(1)}) custom-call(s32[3]{0:T(128)S(1)} %pad_add_fusion.refs_0_, s32[32]{0:T(128)S(1)} %bitcast.11, s32[32]{0:T(128)S(1)} %bitcast.12, bf16[32,128,128]{2,1,0:T(8,128)(2,1)S(1)} %bitcast.5), custom_call_target="tpu_custom_call" | custom-call | flops 33554432 | bytes 1048844 | tf_op jit(solution)/shard_map/pallas_call | solution.py:25
  14.9 0.8 collective-permute-start.9
  17.8 1.1 %shard_map.61 = (f32[8,64,128]{2,1,0:T(8,128)S(1)}, bf16[528,128]{1,0:T(8,128)(2,1)S(1)}, bf16[528,128]{1,0:T(8,128)(2,1)S(1)}, bf16[528,128]{1,0:T(8,128)(2,1)S(1)}) custom-call(s32[3,32]{1,0:T(4,128)S(1)} %get-tuple-element.38.refs_0_.refs_1_, bf16[32,128,128]{2,1,0:T(8,128)(2,1)S(1)} %bitcast.6, bf16[8,64,128]{2,1,0:T(8,128)(2,1)S(1)} %shard_map.60.refs_2_.refs_3_, ...), custom_call_target="tpu_custom_call" | custom-call | flops 67108864 | bytes 2113920 | tf_op jit(solution)/shard_map/pallas_call | solution.py:25
  18.9 1.2 %collective-permute-done.9.refs_6_ = bf16[9,64,128]{2,1,0:T(8,128)(2,1)S(1)} collective-permute-done((bf16[9,64,128]{2,1,0:T(8,128)(2,1)S(1)}, bf16[9,64,128]{2,1,0:T(8,128)(2,1)S(1)}, u32[]{:S(2)}, u32[]{:S(2)}) %collective-permute-start.9) | collective-permute-done | bytes 147488 | tf_op jit(solution)/shard_map/ppermute | solution.py:38
  20.1 1.5 %shard_map.62 = (f32[4,8,64,128]{3,2,1,0:T(8,128)S(1)}, bf16[4,528,128]{2,1,0:T(8,128)(2,1)S(1)}) custom-call(f32[8,64,128]{2,1,0:T(8,128)S(1)} %get-tuple-element.40.refs_0_.refs_4_, s32[3,32]{1,0:T(4,128)S(1)} %get-tuple-element.38.refs_0_.refs_1_, bf16[32,128,128]{2,1,0:T(8,128)(2,1)S(1)} %bitcast.7, bf16[8,64,128]{2,1,0:T(8,128)(2,1)S(1)} %shard_map.60.refs_2_.refs_3_, ...), custom_call_target="tpu_custom_call" | custom-call | flops 67108864 | bytes 1606016 | tf_op jit(solution)/shard_map/pallas_call | solution.py:25
  21.7 0.8 collective-permute-start.14
  22.5 2.0 %collective-permute-start.15 = (bf16[528,128]{1,0:T(8,128)(2,1)S(1)}, bf16[528,128]{1,0:T(8,128)(2,1)S(1)}, u32[]{:S(2)}, u32[]{:S(2)}) collective-permute-start(bf16[528,128]{1,0:T(8,128)(2,1)S(1)} %get-tuple-element.52), channel_id=1, source_target_pairs={{0,16},{8,24},{16,0},{24,8},{1,17},{9,25},{17,1},{25,9},{2,18},{10... | collective-permute-start | bytes 405512 | tf_op jit(solution)/shard_map/ppermute | solution.py:38
  24.6 1.6 %collective-permute-start.16 = (bf16[528,128]{1,0:T(8,128)(2,1)S(1)}, bf16[528,128]{1,0:T(8,128)(2,1)S(1)}, u32[]{:S(2)}, u32[]{:S(2)}) collective-permute-start(bf16[528,128]{1,0:T(8,128)(2,1)S(1)} %get-tuple-element.53), channel_id=1, source_target_pairs={{0,24},{8,16},{16,8},{24,0},{1,25},{9,17},{17,9},{25,1},{2,26},{10... | collective-permute-start | bytes 405512 | tf_op jit(solution)/shard_map/ppermute | solution.py:38
  26.3 1.6 %collective-permute-start.11 = (bf16[528,128]{1,0:T(8,128)(2,1)S(1)}, bf16[528,128]{1,0:T(8,128)(2,1)S(1)}, u32[]{:S(2)}, u32[]{:S(2)}) collective-permute-start(bf16[528,128]{1,0:T(8,128)(2,1)S(1)} %get-tuple-element.48), channel_id=1, source_target_pairs={{0,2},{1,3},{2,0},{3,1},{4,6},{5,7},{6,4},{7,5},{8,10},{9,11},{10,... | collective-permute-start | bytes 405512 | tf_op jit(solution)/shard_map/ppermute | solution.py:38
  27.9 1.5 %collective-permute-start.12 = (bf16[528,128]{1,0:T(8,128)(2,1)S(1)}, bf16[528,128]{1,0:T(8,128)(2,1)S(1)}, u32[]{:S(2)}, u32[]{:S(2)}) collective-permute-start(bf16[528,128]{1,0:T(8,128)(2,1)S(1)} %get-tuple-element.49), channel_id=1, source_target_pairs={{0,4},{1,5},{2,6},{3,7},{4,0},{5,1},{6,2},{7,3},{8,12},{9,13},{10,... | collective-permute-start | bytes 405512 | tf_op jit(solution)/shard_map/ppermute | solution.py:38
  29.8 2.4 %collective-permute-start.13 = (bf16[528,128]{1,0:T(8,128)(2,1)S(1)}, bf16[528,128]{1,0:T(8,128)(2,1)S(1)}, u32[]{:S(2)}, u32[]{:S(2)}) collective-permute-start(bf16[528,128]{1,0:T(8,128)(2,1)S(1)} %get-tuple-element.50), channel_id=1, source_target_pairs={{0,6},{1,7},{2,4},{3,5},{4,2},{5,3},{6,0},{7,1},{8,14},{9,15},{10,... | collective-permute-start | bytes 405512 | tf_op jit(solution)/shard_map/ppermute | solution.py:38
  32.2 3.5 %collective-permute-done.15.refs_9_ = bf16[528,128]{1,0:T(8,128)(2,1)S(1)} collective-permute-done((bf16[528,128]{1,0:T(8,128)(2,1)S(1)}, bf16[528,128]{1,0:T(8,128)(2,1)S(1)}, u32[]{:S(2)}, u32[]{:S(2)}) %collective-permute-start.15) | collective-permute-done | bytes 135200 | tf_op jit(solution)/shard_map/ppermute | solution.py:38
  36.0 2.9 %collective-permute-start.25 = (bf16[8,64,128]{2,1,0:T(8,128)(2,1)S(1)}, bf16[8,64,128]{2,1,0:T(8,128)(2,1)S(1)}, u32[]{:S(2)}, u32[]{:S(2)}) collective-permute-start(bf16[8,64,128]{2,1,0:T(8,128)(2,1)S(1)} %get-tuple-element.56.refs_2_.refs_3_), channel_id=1, source_target_pairs={{0,16},{8,24},{16,0},{24,8},{1,17},{9,25},{17,1},{25,9},{2,18},{10... | collective-permute-start | bytes 393224 | tf_op jit(solution)/shard_map/ppermute | solution.py:38
  39.1 2.4 %collective-permute-start.19 = (bf16[8,64,128]{2,1,0:T(8,128)(2,1)S(1)}, bf16[8,64,128]{2,1,0:T(8,128)(2,1)S(1)}, u32[]{:S(2)}, u32[]{:S(2)}) collective-permute-start(bf16[8,64,128]{2,1,0:T(8,128)(2,1)S(1)} %get-tuple-element.56.refs_2_.refs_3_), channel_id=1, source_target_pairs={{0,6},{1,7},{2,4},{3,5},{4,2},{5,3},{6,0},{7,1},{8,14},{9,15},{10,... | collective-permute-start | bytes 393224 | tf_op jit(solution)/shard_map/ppermute | solution.py:38
  42.6 2.0 %collective-permute-done.24.refs_5_ = bf16[7,64,128]{2,1,0:T(8,128)(2,1)S(1)} collective-permute-done((bf16[7,64,128]{2,1,0:T(8,128)(2,1)S(1)}, bf16[7,64,128]{2,1,0:T(8,128)(2,1)S(1)}, u32[]{:S(2)}, u32[]{:S(2)}) %collective-permute-start.24) | collective-permute-done | bytes 114720 | tf_op jit(solution)/shard_map/ppermute | solution.py:38
  44.6 1.6 %collective-permute-start.26 = (bf16[9,64,128]{2,1,0:T(8,128)(2,1)S(1)}, bf16[9,64,128]{2,1,0:T(8,128)(2,1)S(1)}, u32[]{:S(2)}, u32[]{:S(2)}) collective-permute-start(bf16[9,64,128]{2,1,0:T(8,128)(2,1)S(1)} %pad_maximum_fusion.1), channel_id=1, source_target_pairs={{0,8},{8,0},{16,24},{24,16},{1,9},{9,1},{17,25},{25,17},{2,10},{10... | collective-permute-start | bytes 442376 | tf_op jit(solution)/shard_map/ppermute | solution.py:38
  47.8 0.8 collective-permute-done.22.refs_8_
  48.8 1.1 %shard_map.65 = (f32[8,64,128]{2,1,0:T(8,128)S(1)}, bf16[512,128]{1,0:T(8,128)(2,1)S(1)}, bf16[512,128]{1,0:T(8,128)(2,1)S(1)}, bf16[512,128]{1,0:T(8,128)(2,1)S(1)}) custom-call(s32[3,32]{1,0:T(4,128)S(1)} %get-tuple-element.38.refs_0_.refs_1_, bf16[32,128,128]{2,1,0:T(8,128)(2,1)S(1)} %bitcast.8, ...), custom_call_target="tpu_custom_call" | custom-call | flops 67108864 | bytes 2097536 | tf_op jit(solution)/shard_map/pallas_call | solution.py:25
  49.9 1.5 %shard_map.66 = (f32[4,8,64,128]{3,2,1,0:T(8,128)S(1)}, bf16[4,512,128]{2,1,0:T(8,128)(2,1)S(1)}) custom-call(f32[8,64,128]{2,1,0:T(8,128)S(1)} %get-tuple-element.57.refs_0_.refs_4_, s32[3,32]{1,0:T(4,128)S(1)} %get-tuple-element.38.refs_0_.refs_1_, bf16[32,128,128]{2,1,0:T(8,128)(2,1)S(1)} %bitcast.9, ...), custom_call_target="tpu_custom_call" | custom-call | flops 67108864 | bytes 1573248 | tf_op jit(solution)/shard_map/pallas_call | solution.py:25
  51.8 1.8 %collective-permute-start.31 = (bf16[512,128]{1,0:T(8,128)(2,1)S(1)}, bf16[512,128]{1,0:T(8,128)(2,1)S(1)}, u32[]{:S(2)}, u32[]{:S(2)}) collective-permute-start(bf16[512,128]{1,0:T(8,128)(2,1)S(1)} %get-tuple-element.66), channel_id=1, source_target_pairs={{0,8},{8,0},{16,24},{24,16},{1,9},{9,1},{17,25},{25,17},{2,10},{10... | collective-permute-start | bytes 393224 | tf_op jit(solution)/shard_map/ppermute | solution.py:38
  53.6 0.9 collective-permute-start.32
  54.5 1.7 %collective-permute-start.33 = (bf16[512,128]{1,0:T(8,128)(2,1)S(1)}, bf16[512,128]{1,0:T(8,128)(2,1)S(1)}, u32[]{:S(2)}, u32[]{:S(2)}) collective-permute-start(bf16[512,128]{1,0:T(8,128)(2,1)S(1)} %get-tuple-element.68), channel_id=1, source_target_pairs={{0,24},{8,16},{16,8},{24,0},{1,25},{9,17},{17,9},{25,1},{2,26},{10... | collective-permute-start | bytes 393224 | tf_op jit(solution)/shard_map/ppermute | solution.py:38
  56.3 1.6 %collective-permute-start.28 = (bf16[512,128]{1,0:T(8,128)(2,1)S(1)}, bf16[512,128]{1,0:T(8,128)(2,1)S(1)}, u32[]{:S(2)}, u32[]{:S(2)}) collective-permute-start(bf16[512,128]{1,0:T(8,128)(2,1)S(1)} %get-tuple-element.63), channel_id=1, source_target_pairs={{0,2},{1,3},{2,0},{3,1},{4,6},{5,7},{6,4},{7,5},{8,10},{9,11},{10,... | collective-permute-start | bytes 393224 | tf_op jit(solution)/shard_map/ppermute | solution.py:38
  57.9 1.2 %collective-permute-start.29 = (bf16[512,128]{1,0:T(8,128)(2,1)S(1)}, bf16[512,128]{1,0:T(8,128)(2,1)S(1)}, u32[]{:S(2)}, u32[]{:S(2)}) collective-permute-start(bf16[512,128]{1,0:T(8,128)(2,1)S(1)} %get-tuple-element.64), channel_id=1, source_target_pairs={{0,4},{1,5},{2,6},{3,7},{4,0},{5,1},{6,2},{7,3},{8,12},{9,13},{10,... | collective-permute-start | bytes 393224 | tf_op jit(solution)/shard_map/ppermute | solution.py:38
  59.2 2.8 %collective-permute-start.30 = (bf16[512,128]{1,0:T(8,128)(2,1)S(1)}, bf16[512,128]{1,0:T(8,128)(2,1)S(1)}, u32[]{:S(2)}, u32[]{:S(2)}) collective-permute-start(bf16[512,128]{1,0:T(8,128)(2,1)S(1)} %get-tuple-element.65), channel_id=1, source_target_pairs={{0,6},{1,7},{2,4},{3,5},{4,2},{5,3},{6,0},{7,1},{8,14},{9,15},{10,... | collective-permute-start | bytes 393224 | tf_op jit(solution)/shard_map/ppermute | solution.py:38
  62.0 4.5 %collective-permute-done.32.refs_9_ = bf16[512,128]{1,0:T(8,128)(2,1)S(1)} collective-permute-done((bf16[512,128]{1,0:T(8,128)(2,1)S(1)}, bf16[512,128]{1,0:T(8,128)(2,1)S(1)}, u32[]{:S(2)}, u32[]{:S(2)}) %collective-permute-start.32) | collective-permute-done | bytes 131104 | tf_op jit(solution)/shard_map/ppermute | solution.py:38
  67.3 3.0 %collective-permute-start.42 = (bf16[8,64,128]{2,1,0:T(8,128)(2,1)S(1)}, bf16[8,64,128]{2,1,0:T(8,128)(2,1)S(1)}, u32[]{:S(2)}, u32[]{:S(2)}) collective-permute-start(bf16[8,64,128]{2,1,0:T(8,128)(2,1)S(1)} %get-tuple-element.70.refs_2_.refs_3_), channel_id=1, source_target_pairs={{0,16},{8,24},{16,0},{24,8},{1,17},{9,25},{17,1},{25,9},{2,18},{10... | collective-permute-start | bytes 393224 | tf_op jit(solution)/shard_map/ppermute | solution.py:38
  70.4 2.3 %collective-permute-start.36 = (bf16[8,64,128]{2,1,0:T(8,128)(2,1)S(1)}, bf16[8,64,128]{2,1,0:T(8,128)(2,1)S(1)}, u32[]{:S(2)}, u32[]{:S(2)}) collective-permute-start(bf16[8,64,128]{2,1,0:T(8,128)(2,1)S(1)} %get-tuple-element.70.refs_2_.refs_3_), channel_id=1, source_target_pairs={{0,6},{1,7},{2,4},{3,5},{4,2},{5,3},{6,0},{7,1},{8,14},{9,15},{10,... | collective-permute-start | bytes 393224 | tf_op jit(solution)/shard_map/ppermute | solution.py:38
  73.9 1.9 %collective-permute-done.41.refs_5_ = bf16[7,64,128]{2,1,0:T(8,128)(2,1)S(1)} collective-permute-done((bf16[7,64,128]{2,1,0:T(8,128)(2,1)S(1)}, bf16[7,64,128]{2,1,0:T(8,128)(2,1)S(1)}, u32[]{:S(2)}, u32[]{:S(2)}) %collective-permute-start.41) | collective-permute-done | bytes 114720 | tf_op jit(solution)/shard_map/ppermute | solution.py:38
  75.9 1.4 %collective-permute-start.43 = (bf16[9,64,128]{2,1,0:T(8,128)(2,1)S(1)}, bf16[9,64,128]{2,1,0:T(8,128)(2,1)S(1)}, u32[]{:S(2)}, u32[]{:S(2)}) collective-permute-start(bf16[9,64,128]{2,1,0:T(8,128)(2,1)S(1)} %pad_maximum_fusion.2), channel_id=1, source_target_pairs={{0,8},{8,0},{16,24},{24,16},{1,9},{9,1},{17,25},{25,17},{2,10},{10... | collective-permute-start | bytes 442376 | tf_op jit(solution)/shard_map/ppermute | solution.py:38
  78.9 0.8 collective-permute-done.39.refs_8_
  79.9 1.0 %shard_map.69.refs_1_ = bf16[64,4096]{1,0:T(8,128)(2,1)S(1)} custom-call(s32[3,32]{1,0:T(4,128)S(1)} %get-tuple-element.38.refs_0_.refs_1_, bf16[32,128,128]{2,1,0:T(8,128)(2,1)S(1)} %bitcast.10, bf16[8,64,128]{2,1,0:T(8,128)(2,1)S(1)} %get-tuple-element.70.refs_2_.refs_3_, bf16[8,64,128]{2,1,0:T(8,128)(2,1)S(1)} %collective-permute-done.34.refs_3_, ...), custom_call_target="tpu_custom_call" | custom-call | flops 67108864 | bytes 2097536 | tf_op jit(solution)/shard_map/pallas_call | solution.py:25
  81.1 1.2 %shard_map.70 = f32[40,128]{1,0:T(8,128)S(1)} custom-call(s32[3,32]{1,0:T(4,128)S(1)} %get-tuple-element.38.refs_0_.refs_1_, bf16[64,4096]{1,0:T(8,128)(2,1)S(1)} %shard_map.69.refs_1_, f32[64,128]{1,0:T(8,128)S(1)} %get-tuple-element.71.refs_2_, bf16[8,64,128]{2,1,0:T(8,128)(2,1)S(1)} %get-tuple-element.70.refs_2_.refs_3_, ...), custom_call_target="tpu_custom_call" | custom-call | flops 33554432 | bytes 1081728 | tf_op jit(solution)/shard_map/pallas_call | solution.py:25
  82.5 1.0 %collective-permute-done.44 = f32[40,128]{1,0:T(8,128)S(1)} collective-permute-done((f32[40,128]{1,0:T(8,128)S(1)}, f32[40,128]{1,0:T(8,128)S(1)}, u32[]{:S(2)}, u32[]{:S(2)}) %collective-permute-start.44) | collective-permute-done | bytes 20512 | tf_op jit(solution)/shard_map/ppermute | solution.py:38
  83.6 2.4 %collective-permute-start.47 = (f32[40,128]{1,0:T(8,128)S(1)}, f32[40,128]{1,0:T(8,128)S(1)}, u32[]{:S(2)}, u32[]{:S(2)}) collective-permute-start(f32[40,128]{1,0:T(8,128)S(1)} %add.12), channel_id=1, source_target_pairs={{0,6},{1,7},{2,4},{3,5},{4,2},{5,3},{6,0},{7,1},{8,14},{9,15},{10,... | collective-permute-start | bytes 61448 | tf_op jit(solution)/shard_map/ppermute | solution.py:38
  87.1 1.2 %collective-permute-done.47 = f32[40,128]{1,0:T(8,128)S(1)} collective-permute-done((f32[40,128]{1,0:T(8,128)S(1)}, f32[40,128]{1,0:T(8,128)S(1)}, u32[]{:S(2)}, u32[]{:S(2)}) %collective-permute-start.47) | collective-permute-done | bytes 20512 | tf_op jit(solution)/shard_map/ppermute | solution.py:38
  88.3 1.5 %collective-permute-done.46 = f32[40,128]{1,0:T(8,128)S(1)} collective-permute-done((f32[40,128]{1,0:T(8,128)S(1)}, f32[40,128]{1,0:T(8,128)S(1)}, u32[]{:S(2)}, u32[]{:S(2)}) %collective-permute-start.46) | collective-permute-done | bytes 20512 | tf_op jit(solution)/shard_map/ppermute | solution.py:38
  90.2 2.2 %collective-permute-start.50 = (f32[40,128]{1,0:T(8,128)S(1)}, f32[40,128]{1,0:T(8,128)S(1)}, u32[]{:S(2)}, u32[]{:S(2)}) collective-permute-start(f32[40,128]{1,0:T(8,128)S(1)} %add_add_fusion.refs_1_), channel_id=1, source_target_pairs={{0,24},{8,16},{16,8},{24,0},{1,25},{9,17},{17,9},{25,1},{2,26},{10... | collective-permute-start | bytes 61448 | tf_op jit(solution)/shard_map/ppermute | solution.py:38
  92.4 0.9 collective-permute-start.49
  93.3 1.4 %collective-permute-start.48 = (f32[40,128]{1,0:T(8,128)S(1)}, f32[40,128]{1,0:T(8,128)S(1)}, u32[]{:S(2)}, u32[]{:S(2)}) collective-permute-start(f32[40,128]{1,0:T(8,128)S(1)} %add_add_fusion.refs_1_), channel_id=1, source_target_pairs={{0,8},{8,0},{16,24},{24,16},{1,9},{9,1},{17,25},{25,17},{2,10},{10... | collective-permute-start | bytes 61448 | tf_op jit(solution)/shard_map/ppermute | solution.py:38
  94.7 1.2 %collective-permute-done.50.refs_4_ = f32[40,128]{1,0:T(8,128)S(1)} collective-permute-done((f32[40,128]{1,0:T(8,128)S(1)}, f32[40,128]{1,0:T(8,128)S(1)}, u32[]{:S(2)}, u32[]{:S(2)}) %collective-permute-start.50) | collective-permute-done | bytes 20512 | tf_op jit(solution)/shard_map/ppermute | solution.py:38
  95.9 1.3 %collective-permute-done.49.refs_3_ = f32[40,128]{1,0:T(8,128)S(1)} collective-permute-done((f32[40,128]{1,0:T(8,128)S(1)}, f32[40,128]{1,0:T(8,128)S(1)}, u32[]{:S(2)}, u32[]{:S(2)}) %collective-permute-start.49) | collective-permute-done | bytes 20512 | tf_op jit(solution)/shard_map/ppermute | solution.py:38
  97.3 3.8 %shard_map.71 = (f32[64,1024]{1,0:T(8,128)}, f32[64,64]{1,0:T(8,128)}) custom-call(f32[64,1024]{1,0:T(8,128)S(1)} %get-tuple-element.69.refs_0_, f32[40,128]{1,0:T(8,128)S(1)} %add_add_fusion.refs_1_, f32[40,128]{1,0:T(8,128)S(1)} %collective-permute-done.48.refs_2_, f32[40,128]{1,0:T(8,128)S(1)} %collective-permute-done.49.refs_3_, ...), custom_call_target="tpu_custom_call" | custom-call | bytes 344064 | tf_op jit(solution)/shard_map/pallas_call | solution.py:25
  (91 shorter events, 14.3 us)
Async XLA Ops:
  1.6 13.3 %collective-permute-start.8 = (bf16[8,64,128]{2,1,0:T(8,128)(2,1)S(1)}, bf16[8,64,128]{2,1,0:T(8,128)(2,1)S(1)}, u32[]{:S(2)}, u32[]{:S(2)}) collective-permute-start(bf16[8,64,128]{2,1,0:T(8,128)(2,1)S(1)} %shard_map.60.refs_2_.refs_3_), channel_id=1, source_target_pairs={{0,16},{8,24},{16,0},{24,8},{1,17},{9,25},{17,1},{25,9},{2,18},{10... | collective-permute-start | bytes 393224 | tf_op jit(solution)/shard_map/ppermute | solution.py:38
  5.7 10.0 %collective-permute-start.2 = (bf16[8,64,128]{2,1,0:T(8,128)(2,1)S(1)}, bf16[8,64,128]{2,1,0:T(8,128)(2,1)S(1)}, u32[]{:S(2)}, u32[]{:S(2)}) collective-permute-start(bf16[8,64,128]{2,1,0:T(8,128)(2,1)S(1)} %shard_map.60.refs_2_.refs_3_), channel_id=1, source_target_pairs={{0,6},{1,7},{2,4},{3,5},{4,2},{5,3},{6,0},{7,1},{8,14},{9,15},{10,... | collective-permute-start | bytes 393224 | tf_op jit(solution)/shard_map/ppermute | solution.py:38
  8.2 8.1 %collective-permute-start.1 = (bf16[8,64,128]{2,1,0:T(8,128)(2,1)S(1)}, bf16[8,64,128]{2,1,0:T(8,128)(2,1)S(1)}, u32[]{:S(2)}, u32[]{:S(2)}) collective-permute-start(bf16[8,64,128]{2,1,0:T(8,128)(2,1)S(1)} %shard_map.60.refs_2_.refs_3_), channel_id=1, source_target_pairs={{0,4},{1,5},{2,6},{3,7},{4,0},{5,1},{6,2},{7,3},{8,12},{9,13},{10,... | collective-permute-start | bytes 393224 | tf_op jit(solution)/shard_map/ppermute | solution.py:38
  8.7 7.7 %collective-permute-start = (bf16[8,64,128]{2,1,0:T(8,128)(2,1)S(1)}, bf16[8,64,128]{2,1,0:T(8,128)(2,1)S(1)}, u32[]{:S(2)}, u32[]{:S(2)}) collective-permute-start(bf16[8,64,128]{2,1,0:T(8,128)(2,1)S(1)} %shard_map.60.refs_2_.refs_3_), channel_id=1, source_target_pairs={{0,2},{1,3},{2,0},{3,1},{4,6},{5,7},{6,4},{7,5},{8,10},{9,11},{10,... | collective-permute-start | bytes 393224 | tf_op jit(solution)/shard_map/ppermute | solution.py:38
  9.2 5.7 %collective-permute-start.7 = (bf16[7,64,128]{2,1,0:T(8,128)(2,1)S(1)}, bf16[7,64,128]{2,1,0:T(8,128)(2,1)S(1)}, u32[]{:S(2)}, u32[]{:S(2)}) collective-permute-start(bf16[7,64,128]{2,1,0:T(8,128)(2,1)S(1)} %slice.24), channel_id=1, source_target_pairs={{0,8},{8,0},{16,24},{24,16},{1,9},{9,1},{17,25},{25,17},{2,10},{10... | collective-permute-start | bytes 344072 | tf_op jit(solution)/shard_map/ppermute | solution.py:38
  14.9 5.2 %collective-permute-start.9 = (bf16[9,64,128]{2,1,0:T(8,128)(2,1)S(1)}, bf16[9,64,128]{2,1,0:T(8,128)(2,1)S(1)}, u32[]{:S(2)}, u32[]{:S(2)}) collective-permute-start(bf16[9,64,128]{2,1,0:T(8,128)(2,1)S(1)} %pad_maximum_fusion), channel_id=1, source_target_pairs={{0,8},{8,0},{16,24},{24,16},{1,9},{9,1},{17,25},{25,17},{2,10},{10... | collective-permute-start | bytes 442376 | tf_op jit(solution)/shard_map/ppermute | solution.py:38
  15.7 1.3 %collective-permute-start.3 = (bf16[8,64,128]{2,1,0:T(8,128)(2,1)S(1)}, bf16[8,64,128]{2,1,0:T(8,128)(2,1)S(1)}, u32[]{:S(2)}, u32[]{:S(2)}) collective-permute-start(bf16[8,64,128]{2,1,0:T(8,128)(2,1)S(1)} %shard_map.60.refs_2_.refs_3_), channel_id=1, source_target_pairs={{0,1},{1,0},{2,3},{3,2},{4,5},{5,4},{6,7},{7,6},{8,9},{9,8},{10,11... | collective-permute-start | bytes 393224 | tf_op jit(solution)/shard_map/ppermute | solution.py:38
  15.7 1.5 %collective-permute-start.6 = (bf16[8,64,128]{2,1,0:T(8,128)(2,1)S(1)}, bf16[8,64,128]{2,1,0:T(8,128)(2,1)S(1)}, u32[]{:S(2)}, u32[]{:S(2)}) collective-permute-start(bf16[8,64,128]{2,1,0:T(8,128)(2,1)S(1)} %collective-permute-done.2.refs_5_), channel_id=1, source_target_pairs={{0,1},{1,0},{2,3},{3,2},{4,5},{5,4},{6,7},{7,6},{8,9},{9,8},{10,11... | collective-permute-start | bytes 393224 | tf_op jit(solution)/shard_map/ppermute | solution.py:38
  16.2 1.3 %collective-permute-start.5 = (bf16[8,64,128]{2,1,0:T(8,128)(2,1)S(1)}, bf16[8,64,128]{2,1,0:T(8,128)(2,1)S(1)}, u32[]{:S(2)}, u32[]{:S(2)}) collective-permute-start(bf16[8,64,128]{2,1,0:T(8,128)(2,1)S(1)} %collective-permute-done.1.refs_4_), channel_id=1, source_target_pairs={{0,1},{1,0},{2,3},{3,2},{4,5},{5,4},{6,7},{7,6},{8,9},{9,8},{10,11... | collective-permute-start | bytes 393224 | tf_op jit(solution)/shard_map/ppermute | solution.py:38
  16.3 1.5 %collective-permute-start.4 = (bf16[8,64,128]{2,1,0:T(8,128)(2,1)S(1)}, bf16[8,64,128]{2,1,0:T(8,128)(2,1)S(1)}, u32[]{:S(2)}, u32[]{:S(2)}) collective-permute-start(bf16[8,64,128]{2,1,0:T(8,128)(2,1)S(1)} %collective-permute-done.refs_3_), channel_id=1, source_target_pairs={{0,1},{1,0},{2,3},{3,2},{4,5},{5,4},{6,7},{7,6},{8,9},{9,8},{10,11... | collective-permute-start | bytes 393224 | tf_op jit(solution)/shard_map/ppermute | solution.py:38
  21.7 4.5 %collective-permute-start.10 = (bf16[4,528,128]{2,1,0:T(8,128)(2,1)S(1)}, bf16[4,528,128]{2,1,0:T(8,128)(2,1)S(1)}, u32[]{:S(2)}, u32[]{:S(2)}) collective-permute-start(bf16[4,528,128]{2,1,0:T(8,128)(2,1)S(1)} %get-tuple-element.45), channel_id=1, source_target_pairs={{0,1},{1,0},{2,3},{3,2},{4,5},{5,4},{6,7},{7,6},{8,9},{9,8},{10,11... | collective-permute-start | bytes 1622024 | tf_op jit(solution)/shard_map/ppermute | solution.py:38
  21.7 8.1 %collective-permute-start.14 = (bf16[528,128]{1,0:T(8,128)(2,1)S(1)}, bf16[528,128]{1,0:T(8,128)(2,1)S(1)}, u32[]{:S(2)}, u32[]{:S(2)}) collective-permute-start(bf16[528,128]{1,0:T(8,128)(2,1)S(1)} %get-tuple-element.51), channel_id=1, source_target_pairs={{0,8},{8,0},{16,24},{24,16},{1,9},{9,1},{17,25},{25,17},{2,10},{10... | collective-permute-start | bytes 405512 | tf_op jit(solution)/shard_map/ppermute | solution.py:38
  22.5 13.2 %collective-permute-start.15 = (bf16[528,128]{1,0:T(8,128)(2,1)S(1)}, bf16[528,128]{1,0:T(8,128)(2,1)S(1)}, u32[]{:S(2)}, u32[]{:S(2)}) collective-permute-start(bf16[528,128]{1,0:T(8,128)(2,1)S(1)} %get-tuple-element.52), channel_id=1, source_target_pairs={{0,16},{8,24},{16,0},{24,8},{1,17},{9,25},{17,1},{25,9},{2,18},{10... | collective-permute-start | bytes 405512 | tf_op jit(solution)/shard_map/ppermute | solution.py:38
  24.6 11.1 %collective-permute-start.16 = (bf16[528,128]{1,0:T(8,128)(2,1)S(1)}, bf16[528,128]{1,0:T(8,128)(2,1)S(1)}, u32[]{:S(2)}, u32[]{:S(2)}) collective-permute-start(bf16[528,128]{1,0:T(8,128)(2,1)S(1)} %get-tuple-element.53), channel_id=1, source_target_pairs={{0,24},{8,16},{16,8},{24,0},{1,25},{9,17},{17,9},{25,1},{2,26},{10... | collective-permute-start | bytes 405512 | tf_op jit(solution)/shard_map/ppermute | solution.py:38
  26.3 9.4 %collective-permute-start.11 = (bf16[528,128]{1,0:T(8,128)(2,1)S(1)}, bf16[528,128]{1,0:T(8,128)(2,1)S(1)}, u32[]{:S(2)}, u32[]{:S(2)}) collective-permute-start(bf16[528,128]{1,0:T(8,128)(2,1)S(1)} %get-tuple-element.48), channel_id=1, source_target_pairs={{0,2},{1,3},{2,0},{3,1},{4,6},{5,7},{6,4},{7,5},{8,10},{9,11},{10,... | collective-permute-start | bytes 405512 | tf_op jit(solution)/shard_map/ppermute | solution.py:38
  27.9 7.9 %collective-permute-start.12 = (bf16[528,128]{1,0:T(8,128)(2,1)S(1)}, bf16[528,128]{1,0:T(8,128)(2,1)S(1)}, u32[]{:S(2)}, u32[]{:S(2)}) collective-permute-start(bf16[528,128]{1,0:T(8,128)(2,1)S(1)} %get-tuple-element.49), channel_id=1, source_target_pairs={{0,4},{1,5},{2,6},{3,7},{4,0},{5,1},{6,2},{7,3},{8,12},{9,13},{10,... | collective-permute-start | bytes 405512 | tf_op jit(solution)/shard_map/ppermute | solution.py:38
  29.8 6.0 %collective-permute-start.13 = (bf16[528,128]{1,0:T(8,128)(2,1)S(1)}, bf16[528,128]{1,0:T(8,128)(2,1)S(1)}, u32[]{:S(2)}, u32[]{:S(2)}) collective-permute-start(bf16[528,128]{1,0:T(8,128)(2,1)S(1)} %get-tuple-element.50), channel_id=1, source_target_pairs={{0,6},{1,7},{2,4},{3,5},{4,2},{5,3},{6,0},{7,1},{8,14},{9,15},{10,... | collective-permute-start | bytes 405512 | tf_op jit(solution)/shard_map/ppermute | solution.py:38
  36.0 8.6 %collective-permute-start.25 = (bf16[8,64,128]{2,1,0:T(8,128)(2,1)S(1)}, bf16[8,64,128]{2,1,0:T(8,128)(2,1)S(1)}, u32[]{:S(2)}, u32[]{:S(2)}) collective-permute-start(bf16[8,64,128]{2,1,0:T(8,128)(2,1)S(1)} %get-tuple-element.56.refs_2_.refs_3_), channel_id=1, source_target_pairs={{0,16},{8,24},{16,0},{24,8},{1,17},{9,25},{17,1},{25,9},{2,18},{10... | collective-permute-start | bytes 393224 | tf_op jit(solution)/shard_map/ppermute | solution.py:38
  39.0 5.6 %collective-permute-start.24 = (bf16[7,64,128]{2,1,0:T(8,128)(2,1)S(1)}, bf16[7,64,128]{2,1,0:T(8,128)(2,1)S(1)}, u32[]{:S(2)}, u32[]{:S(2)}) collective-permute-start(bf16[7,64,128]{2,1,0:T(8,128)(2,1)S(1)} %slice.20), channel_id=1, source_target_pairs={{0,8},{8,0},{16,24},{24,16},{1,9},{9,1},{17,25},{25,17},{2,10},{10... | collective-permute-start | bytes 344072 | tf_op jit(solution)/shard_map/ppermute | solution.py:38
  39.1 7.1 %collective-permute-start.19 = (bf16[8,64,128]{2,1,0:T(8,128)(2,1)S(1)}, bf16[8,64,128]{2,1,0:T(8,128)(2,1)S(1)}, u32[]{:S(2)}, u32[]{:S(2)}) collective-permute-start(bf16[8,64,128]{2,1,0:T(8,128)(2,1)S(1)} %get-tuple-element.56.refs_2_.refs_3_), channel_id=1, source_target_pairs={{0,6},{1,7},{2,4},{3,5},{4,2},{5,3},{6,0},{7,1},{8,14},{9,15},{10,... | collective-permute-start | bytes 393224 | tf_op jit(solution)/shard_map/ppermute | solution.py:38
  41.6 5.7 %collective-permute-start.18 = (bf16[8,64,128]{2,1,0:T(8,128)(2,1)S(1)}, bf16[8,64,128]{2,1,0:T(8,128)(2,1)S(1)}, u32[]{:S(2)}, u32[]{:S(2)}) collective-permute-start(bf16[8,64,128]{2,1,0:T(8,128)(2,1)S(1)} %get-tuple-element.56.refs_2_.refs_3_), channel_id=1, source_target_pairs={{0,4},{1,5},{2,6},{3,7},{4,0},{5,1},{6,2},{7,3},{8,12},{9,13},{10,... | collective-permute-start | bytes 393224 | tf_op jit(solution)/shard_map/ppermute | solution.py:38
  42.1 5.2 %collective-permute-start.17 = (bf16[8,64,128]{2,1,0:T(8,128)(2,1)S(1)}, bf16[8,64,128]{2,1,0:T(8,128)(2,1)S(1)}, u32[]{:S(2)}, u32[]{:S(2)}) collective-permute-start(bf16[8,64,128]{2,1,0:T(8,128)(2,1)S(1)} %get-tuple-element.56.refs_2_.refs_3_), channel_id=1, source_target_pairs={{0,2},{1,3},{2,0},{3,1},{4,6},{5,7},{6,4},{7,5},{8,10},{9,11},{10,... | collective-permute-start | bytes 393224 | tf_op jit(solution)/shard_map/ppermute | solution.py:38
  44.6 5.3 %collective-permute-start.26 = (bf16[9,64,128]{2,1,0:T(8,128)(2,1)S(1)}, bf16[9,64,128]{2,1,0:T(8,128)(2,1)S(1)}, u32[]{:S(2)}, u32[]{:S(2)}) collective-permute-start(bf16[9,64,128]{2,1,0:T(8,128)(2,1)S(1)} %pad_maximum_fusion.1), channel_id=1, source_target_pairs={{0,8},{8,0},{16,24},{24,16},{1,9},{9,1},{17,25},{25,17},{2,10},{10... | collective-permute-start | bytes 442376 | tf_op jit(solution)/shard_map/ppermute | solution.py:38
  46.2 1.6 %collective-permute-start.20 = (bf16[8,64,128]{2,1,0:T(8,128)(2,1)S(1)}, bf16[8,64,128]{2,1,0:T(8,128)(2,1)S(1)}, u32[]{:S(2)}, u32[]{:S(2)}) collective-permute-start(bf16[8,64,128]{2,1,0:T(8,128)(2,1)S(1)} %get-tuple-element.56.refs_2_.refs_3_), channel_id=1, source_target_pairs={{0,1},{1,0},{2,3},{3,2},{4,5},{5,4},{6,7},{7,6},{8,9},{9,8},{10,11... | collective-permute-start | bytes 393224 | tf_op jit(solution)/shard_map/ppermute | solution.py:38
  46.2 1.6 %collective-permute-start.23 = (bf16[8,64,128]{2,1,0:T(8,128)(2,1)S(1)}, bf16[8,64,128]{2,1,0:T(8,128)(2,1)S(1)}, u32[]{:S(2)}, u32[]{:S(2)}) collective-permute-start(bf16[8,64,128]{2,1,0:T(8,128)(2,1)S(1)} %collective-permute-done.19.refs_5_), channel_id=1, source_target_pairs={{0,1},{1,0},{2,3},{3,2},{4,5},{5,4},{6,7},{7,6},{8,9},{9,8},{10,11... | collective-permute-start | bytes 393224 | tf_op jit(solution)/shard_map/ppermute | solution.py:38
  47.3 1.4 %collective-permute-start.21 = (bf16[8,64,128]{2,1,0:T(8,128)(2,1)S(1)}, bf16[8,64,128]{2,1,0:T(8,128)(2,1)S(1)}, u32[]{:S(2)}, u32[]{:S(2)}) collective-permute-start(bf16[8,64,128]{2,1,0:T(8,128)(2,1)S(1)} %collective-permute-done.17.refs_3_), channel_id=1, source_target_pairs={{0,1},{1,0},{2,3},{3,2},{4,5},{5,4},{6,7},{7,6},{8,9},{9,8},{10,11... | collective-permute-start | bytes 393224 | tf_op jit(solution)/shard_map/ppermute | solution.py:38
  51.4 4.8 %collective-permute-start.27 = (bf16[4,512,128]{2,1,0:T(8,128)(2,1)S(1)}, bf16[4,512,128]{2,1,0:T(8,128)(2,1)S(1)}, u32[]{:S(2)}, u32[]{:S(2)}) collective-permute-start(bf16[4,512,128]{2,1,0:T(8,128)(2,1)S(1)} %get-tuple-element.61), channel_id=1, source_target_pairs={{0,1},{1,0},{2,3},{3,2},{4,5},{5,4},{6,7},{7,6},{8,9},{9,8},{10,11... | collective-permute-start | bytes 1572872 | tf_op jit(solution)/shard_map/ppermute | solution.py:38
  51.8 7.4 %collective-permute-start.31 = (bf16[512,128]{1,0:T(8,128)(2,1)S(1)}, bf16[512,128]{1,0:T(8,128)(2,1)S(1)}, u32[]{:S(2)}, u32[]{:S(2)}) collective-permute-start(bf16[512,128]{1,0:T(8,128)(2,1)S(1)} %get-tuple-element.66), channel_id=1, source_target_pairs={{0,8},{8,0},{16,24},{24,16},{1,9},{9,1},{17,25},{25,17},{2,10},{10... | collective-permute-start | bytes 393224 | tf_op jit(solution)/shard_map/ppermute | solution.py:38
  53.6 12.9 %collective-permute-start.32 = (bf16[512,128]{1,0:T(8,128)(2,1)S(1)}, bf16[512,128]{1,0:T(8,128)(2,1)S(1)}, u32[]{:S(2)}, u32[]{:S(2)}) collective-permute-start(bf16[512,128]{1,0:T(8,128)(2,1)S(1)} %get-tuple-element.67), channel_id=1, source_target_pairs={{0,16},{8,24},{16,0},{24,8},{1,17},{9,25},{17,1},{25,9},{2,18},{10... | collective-permute-start | bytes 393224 | tf_op jit(solution)/shard_map/ppermute | solution.py:38
  54.5 12.0 %collective-permute-start.33 = (bf16[512,128]{1,0:T(8,128)(2,1)S(1)}, bf16[512,128]{1,0:T(8,128)(2,1)S(1)}, u32[]{:S(2)}, u32[]{:S(2)}) collective-permute-start(bf16[512,128]{1,0:T(8,128)(2,1)S(1)} %get-tuple-element.68), channel_id=1, source_target_pairs={{0,24},{8,16},{16,8},{24,0},{1,25},{9,17},{17,9},{25,1},{2,26},{10... | collective-permute-start | bytes 393224 | tf_op jit(solution)/shard_map/ppermute | solution.py:38
  56.3 10.2 %collective-permute-start.28 = (bf16[512,128]{1,0:T(8,128)(2,1)S(1)}, bf16[512,128]{1,0:T(8,128)(2,1)S(1)}, u32[]{:S(2)}, u32[]{:S(2)}) collective-permute-start(bf16[512,128]{1,0:T(8,128)(2,1)S(1)} %get-tuple-element.63), channel_id=1, source_target_pairs={{0,2},{1,3},{2,0},{3,1},{4,6},{5,7},{6,4},{7,5},{8,10},{9,11},{10,... | collective-permute-start | bytes 393224 | tf_op jit(solution)/shard_map/ppermute | solution.py:38
  57.9 8.6 %collective-permute-start.29 = (bf16[512,128]{1,0:T(8,128)(2,1)S(1)}, bf16[512,128]{1,0:T(8,128)(2,1)S(1)}, u32[]{:S(2)}, u32[]{:S(2)}) collective-permute-start(bf16[512,128]{1,0:T(8,128)(2,1)S(1)} %get-tuple-element.64), channel_id=1, source_target_pairs={{0,4},{1,5},{2,6},{3,7},{4,0},{5,1},{6,2},{7,3},{8,12},{9,13},{10,... | collective-permute-start | bytes 393224 | tf_op jit(solution)/shard_map/ppermute | solution.py:38
  59.2 7.3 %collective-permute-start.30 = (bf16[512,128]{1,0:T(8,128)(2,1)S(1)}, bf16[512,128]{1,0:T(8,128)(2,1)S(1)}, u32[]{:S(2)}, u32[]{:S(2)}) collective-permute-start(bf16[512,128]{1,0:T(8,128)(2,1)S(1)} %get-tuple-element.65), channel_id=1, source_target_pairs={{0,6},{1,7},{2,4},{3,5},{4,2},{5,3},{6,0},{7,1},{8,14},{9,15},{10,... | collective-permute-start | bytes 393224 | tf_op jit(solution)/shard_map/ppermute | solution.py:38
  67.3 8.6 %collective-permute-start.42 = (bf16[8,64,128]{2,1,0:T(8,128)(2,1)S(1)}, bf16[8,64,128]{2,1,0:T(8,128)(2,1)S(1)}, u32[]{:S(2)}, u32[]{:S(2)}) collective-permute-start(bf16[8,64,128]{2,1,0:T(8,128)(2,1)S(1)} %get-tuple-element.70.refs_2_.refs_3_), channel_id=1, source_target_pairs={{0,16},{8,24},{16,0},{24,8},{1,17},{9,25},{17,1},{25,9},{2,18},{10... | collective-permute-start | bytes 393224 | tf_op jit(solution)/shard_map/ppermute | solution.py:38
  70.3 5.5 %collective-permute-start.41 = (bf16[7,64,128]{2,1,0:T(8,128)(2,1)S(1)}, bf16[7,64,128]{2,1,0:T(8,128)(2,1)S(1)}, u32[]{:S(2)}, u32[]{:S(2)}) collective-permute-start(bf16[7,64,128]{2,1,0:T(8,128)(2,1)S(1)} %slice.22), channel_id=1, source_target_pairs={{0,8},{8,0},{16,24},{24,16},{1,9},{9,1},{17,25},{25,17},{2,10},{10... | collective-permute-start | bytes 344072 | tf_op jit(solution)/shard_map/ppermute | solution.py:38
  70.4 7.0 %collective-permute-start.36 = (bf16[8,64,128]{2,1,0:T(8,128)(2,1)S(1)}, bf16[8,64,128]{2,1,0:T(8,128)(2,1)S(1)}, u32[]{:S(2)}, u32[]{:S(2)}) collective-permute-start(bf16[8,64,128]{2,1,0:T(8,128)(2,1)S(1)} %get-tuple-element.70.refs_2_.refs_3_), channel_id=1, source_target_pairs={{0,6},{1,7},{2,4},{3,5},{4,2},{5,3},{6,0},{7,1},{8,14},{9,15},{10,... | collective-permute-start | bytes 393224 | tf_op jit(solution)/shard_map/ppermute | solution.py:38
  72.7 5.7 %collective-permute-start.35 = (bf16[8,64,128]{2,1,0:T(8,128)(2,1)S(1)}, bf16[8,64,128]{2,1,0:T(8,128)(2,1)S(1)}, u32[]{:S(2)}, u32[]{:S(2)}) collective-permute-start(bf16[8,64,128]{2,1,0:T(8,128)(2,1)S(1)} %get-tuple-element.70.refs_2_.refs_3_), channel_id=1, source_target_pairs={{0,4},{1,5},{2,6},{3,7},{4,0},{5,1},{6,2},{7,3},{8,12},{9,13},{10,... | collective-permute-start | bytes 393224 | tf_op jit(solution)/shard_map/ppermute | solution.py:38
  73.3 5.1 %collective-permute-start.34 = (bf16[8,64,128]{2,1,0:T(8,128)(2,1)S(1)}, bf16[8,64,128]{2,1,0:T(8,128)(2,1)S(1)}, u32[]{:S(2)}, u32[]{:S(2)}) collective-permute-start(bf16[8,64,128]{2,1,0:T(8,128)(2,1)S(1)} %get-tuple-element.70.refs_2_.refs_3_), channel_id=1, source_target_pairs={{0,2},{1,3},{2,0},{3,1},{4,6},{5,7},{6,4},{7,5},{8,10},{9,11},{10,... | collective-permute-start | bytes 393224 | tf_op jit(solution)/shard_map/ppermute | solution.py:38
  75.9 5.2 %collective-permute-start.43 = (bf16[9,64,128]{2,1,0:T(8,128)(2,1)S(1)}, bf16[9,64,128]{2,1,0:T(8,128)(2,1)S(1)}, u32[]{:S(2)}, u32[]{:S(2)}) collective-permute-start(bf16[9,64,128]{2,1,0:T(8,128)(2,1)S(1)} %pad_maximum_fusion.2), channel_id=1, source_target_pairs={{0,8},{8,0},{16,24},{24,16},{1,9},{9,1},{17,25},{25,17},{2,10},{10... | collective-permute-start | bytes 442376 | tf_op jit(solution)/shard_map/ppermute | solution.py:38
  77.3 1.6 %collective-permute-start.37 = (bf16[8,64,128]{2,1,0:T(8,128)(2,1)S(1)}, bf16[8,64,128]{2,1,0:T(8,128)(2,1)S(1)}, u32[]{:S(2)}, u32[]{:S(2)}) collective-permute-start(bf16[8,64,128]{2,1,0:T(8,128)(2,1)S(1)} %get-tuple-element.70.refs_2_.refs_3_), channel_id=1, source_target_pairs={{0,1},{1,0},{2,3},{3,2},{4,5},{5,4},{6,7},{7,6},{8,9},{9,8},{10,11... | collective-permute-start | bytes 393224 | tf_op jit(solution)/shard_map/ppermute | solution.py:38
  77.4 1.5 %collective-permute-start.40 = (bf16[8,64,128]{2,1,0:T(8,128)(2,1)S(1)}, bf16[8,64,128]{2,1,0:T(8,128)(2,1)S(1)}, u32[]{:S(2)}, u32[]{:S(2)}) collective-permute-start(bf16[8,64,128]{2,1,0:T(8,128)(2,1)S(1)} %collective-permute-done.36.refs_5_), channel_id=1, source_target_pairs={{0,1},{1,0},{2,3},{3,2},{4,5},{5,4},{6,7},{7,6},{8,9},{9,8},{10,11... | collective-permute-start | bytes 393224 | tf_op jit(solution)/shard_map/ppermute | solution.py:38
  78.4 1.5 %collective-permute-start.38 = (bf16[8,64,128]{2,1,0:T(8,128)(2,1)S(1)}, bf16[8,64,128]{2,1,0:T(8,128)(2,1)S(1)}, u32[]{:S(2)}, u32[]{:S(2)}) collective-permute-start(bf16[8,64,128]{2,1,0:T(8,128)(2,1)S(1)} %collective-permute-done.34.refs_3_), channel_id=1, source_target_pairs={{0,1},{1,0},{2,3},{3,2},{4,5},{5,4},{6,7},{7,6},{8,9},{9,8},{10,11... | collective-permute-start | bytes 393224 | tf_op jit(solution)/shard_map/ppermute | solution.py:38
  83.6 4.7 %collective-permute-start.47 = (f32[40,128]{1,0:T(8,128)S(1)}, f32[40,128]{1,0:T(8,128)S(1)}, u32[]{:S(2)}, u32[]{:S(2)}) collective-permute-start(f32[40,128]{1,0:T(8,128)S(1)} %add.12), channel_id=1, source_target_pairs={{0,6},{1,7},{2,4},{3,5},{4,2},{5,3},{6,0},{7,1},{8,14},{9,15},{10,... | collective-permute-start | bytes 61448 | tf_op jit(solution)/shard_map/ppermute | solution.py:38
  86.0 3.8 %collective-permute-start.46 = (f32[40,128]{1,0:T(8,128)S(1)}, f32[40,128]{1,0:T(8,128)S(1)}, u32[]{:S(2)}, u32[]{:S(2)}) collective-permute-start(f32[40,128]{1,0:T(8,128)S(1)} %add.12), channel_id=1, source_target_pairs={{0,4},{1,5},{2,6},{3,7},{4,0},{5,1},{6,2},{7,3},{8,12},{9,13},{10,... | collective-permute-start | bytes 61448 | tf_op jit(solution)/shard_map/ppermute | solution.py:38
  86.4 3.8 %collective-permute-start.45 = (f32[40,128]{1,0:T(8,128)S(1)}, f32[40,128]{1,0:T(8,128)S(1)}, u32[]{:S(2)}, u32[]{:S(2)}) collective-permute-start(f32[40,128]{1,0:T(8,128)S(1)} %add.12), channel_id=1, source_target_pairs={{0,2},{1,3},{2,0},{3,1},{4,6},{5,7},{6,4},{7,5},{8,10},{9,11},{10,... | collective-permute-start | bytes 61448 | tf_op jit(solution)/shard_map/ppermute | solution.py:38
  90.2 5.6 %collective-permute-start.50 = (f32[40,128]{1,0:T(8,128)S(1)}, f32[40,128]{1,0:T(8,128)S(1)}, u32[]{:S(2)}, u32[]{:S(2)}) collective-permute-start(f32[40,128]{1,0:T(8,128)S(1)} %add_add_fusion.refs_1_), channel_id=1, source_target_pairs={{0,24},{8,16},{16,8},{24,0},{1,25},{9,17},{17,9},{25,1},{2,26},{10... | collective-permute-start | bytes 61448 | tf_op jit(solution)/shard_map/ppermute | solution.py:38
  92.4 4.8 %collective-permute-start.49 = (f32[40,128]{1,0:T(8,128)S(1)}, f32[40,128]{1,0:T(8,128)S(1)}, u32[]{:S(2)}, u32[]{:S(2)}) collective-permute-start(f32[40,128]{1,0:T(8,128)S(1)} %add_add_fusion.refs_1_), channel_id=1, source_target_pairs={{0,16},{8,24},{16,0},{24,8},{1,17},{9,25},{17,1},{25,9},{2,18},{10... | collective-permute-start | bytes 61448 | tf_op jit(solution)/shard_map/ppermute | solution.py:38
  93.3 4.0 %collective-permute-start.48 = (f32[40,128]{1,0:T(8,128)S(1)}, f32[40,128]{1,0:T(8,128)S(1)}, u32[]{:S(2)}, u32[]{:S(2)}) collective-permute-start(f32[40,128]{1,0:T(8,128)S(1)} %add_add_fusion.refs_1_), channel_id=1, source_target_pairs={{0,8},{8,0},{16,24},{24,16},{1,9},{9,1},{17,25},{25,17},{2,10},{10... | collective-permute-start | bytes 61448 | tf_op jit(solution)/shard_map/ppermute | solution.py:38
  (9 other events, 22.0 us)

commit v13 on v12

--- a/solution.py
+++ b/solution.py
@@ -82,9 +82,9 @@
         table[0, t] = (lax.div(col, group) ^ meta[0]) * group + lax.rem(col, group)
         table[1, t] = apart * group + inside
         table[2, t] = halves * group + inside
-        for ref, place, dims in ((row_ref, table[2, t], NT), (col_ref, table[0, t], NN)):
-            sums = lax.dot_general(ones, tiles_ref[t], dims, preferred_element_type=F32)
-            ref[pl.ds(place, 1), :] += sums[:1]
+        sums = lax.dot_general(ones, tiles_ref[t], NT, preferred_element_type=F32)
+        row_ref[pl.ds(table[2, t], 1), :] += sums[:1]
+        col_ref[pl.ds(table[0, t], 1), :] += jnp.sum(tiles_ref[t].astype(F32), 0, keepdims=True)
 
 
 def column_kernel(runs, degree, table, tiles_ref, *refs):
@@ -110,8 +110,9 @@
     parts, refs = refs[: len(runs)], refs[len(runs) :]
     if degree:
         sums, *refs = refs
-    kept_ref, swap_ref, panel, total = refs
-    half, group, vectors_n, _ = kept_ref.shape
+    total, swap_ref, panel = refs
+    half, vectors_n = swap_ref.shape[0], total.shape[1]
+    group = total.shape[0] // (2 * half)
     fill(panel, parts, runs)
     total[...] = jnp.zeros_like(total)
     for t in range(tiles_ref.shape[0]):
@@ -119,7 +120,6 @@
             panel[table[0, t]], tiles_ref[t], NT, preferred_element_type=F32
         )
     for d in range(half):
-        kept_ref[d] = total[d * group : (d + 1) * group]
         round_sums(swap_ref.at[d], total, (half + d) * group, group)
         if degree:
             rows = slice((half + d) * group, (half + d + 1) * group)
@@ -159,10 +159,10 @@
     kept, swap = call(
         functools.partial(row_kernel, runs[0], bool(degree)),
         [
-            jax.ShapeDtypeStruct((half, group, vectors_n, width), F32),
+            jax.ShapeDtypeStruct((2 * half * group, vectors_n, width), F32),
             jax.ShapeDtypeStruct((half, rows, width), BF16),
         ],
-        panels(rows_n, 2 * half),
+        panels(rows_n, 2 * half)[:1],
         24,
         [table, tiles, *col_parts, *degree[:1]],
         flops,
@@ -177,14 +177,14 @@
         row_degree, own_ref, own_degree, *send_refs = refs
     else:
         own_ref, *send_refs = refs
-    _, group, vectors_n, _ = kept.shape
+    group, vectors_n, _ = own_ref.shape
     for k in range(group):
         rows = slice(k * vectors_n, (k + 1) * vectors_n)
-        own_ref[k] = kept[0, k] + got[0, rows, :].astype(F32)
+        own_ref[k] = kept[k] + got[0, rows, :].astype(F32)
         for d, send in enumerate(send_refs, 1):
-            send[rows, :] = (kept[d, k] + got[d, rows, :].astype(F32)).astype(BF16)
+            send[rows, :] = (kept[d * group + k] + got[d, rows, :].astype(F32)).astype(BF16)
     if degree:
-        for d in range(kept.shape[0]):
+        for d in range(got.shape[0]):
             sums = row_degree[d * group : (d + 1) * group, :] + join_degree(got.at[d], group)
             if d:
                 send_refs[d - 1][group * vectors_n :, :] = split_degree(sums)
@@ -193,11 +193,12 @@
 
 
 def merge(kept, got, degree):
-    _, group, _, width = kept.shape
-    out_shape = [jax.ShapeDtypeStruct(kept.shape[1:], F32)]
+    half, (_, vectors_n, width) = got.shape[0], kept.shape
+    group = kept.shape[0] // (2 * half)
+    out_shape = [jax.ShapeDtypeStruct((group, vectors_n, width), F32)]
     if degree:
         out_shape += [jax.ShapeDtypeStruct((group, width), F32)]
-    out_shape += [jax.ShapeDtypeStruct(got.shape[1:], BF16)] * (kept.shape[0] - 1)
+    out_shape += [jax.ShapeDtypeStruct(got.shape[1:], BF16)] * (half - 1)
     kernel = functools.partial(merge_kernel, bool(degree))
     return call(kernel, out_shape, [], 24, [kept, got, *degree[:1]])
 
@@ -233,8 +234,8 @@
 
 def filter_kernel(chips_n, start_ref, first_ref, degree_ref, row_own, col_own, *refs):
     row_refs, refs = refs[: chips_n - 1], refs[chips_n - 1 :]
-    col_refs, (filtered_ref, rounded_ref, gram_ref, both) = refs[:-4], refs[-4:]
-    group, vectors_n, width = rounded_ref.shape
+    col_refs, (filtered_ref, rounded_ref) = refs[:-2], refs[-2:]
+    width = rounded_ref.shape[2]
     for k, vec in enumerate(tiles_first(first_ref, width)):
         symmetric = symmetric_part(row_own, row_refs, col_own, col_refs, k)
         columns = slice(k * width, (k + 1) * width)
@@ -242,8 +243,14 @@
         filtered = 2.0 * (image - CENTER * vec) / HALF_WIDTH - start_ref[:, columns]
         filtered_ref[:, columns] = filtered
         rounded_ref[k] = filtered.astype(BF16)
-        both[:vectors_n, columns] = filtered
-        both[vectors_n:, columns] = degree_ref[k : k + 1, :] * filtered
+
+
+def gram_kernel(filtered_ref, degree_ref, gram_ref, both):
+    vectors_n, width = filtered_ref.shape[0], degree_ref.shape[1]
+    for k, vec in enumerate(tiles_first(filtered_ref, width)):
+        columns = slice(k * width, (k + 1) * width)
+        both[:vectors_n, columns] = vec
+        both[vectors_n:, columns] = degree_ref[k : k + 1, :] * vec
     gram_ref[...] = lax.dot_general(
         filtered_ref[...], both[...], NT, precision=HIGHEST, preferred_element_type=F32
     )
@@ -421,14 +428,22 @@
         24,
         [start, *apply(rounded, tuple(degree))],
     )
-    filtered, rounded, gram = call(
+    filtered, rounded = call(
         functools.partial(filter_kernel, chips_n),
-        [vector_shape, rounded_shape, jax.ShapeDtypeStruct((vectors_n, 2 * vectors_n), F32)],
+        [vector_shape, rounded_shape],
+        [],
+        24,
+        [start, first, degree, *apply(rounded)],
+    )
+    gram = call(
+        gram_kernel,
+        jax.ShapeDtypeStruct((vectors_n, 2 * vectors_n), F32),
         [pltpu.VMEM((2 * vectors_n, own_nodes), F32)],
-        24,
-        [start, first, degree, *apply(rounded)],
-    )
-    col_parts, row_parts = gather(rounded)
+        16,
+        [filtered, degree],
+        24 * vectors_n * vectors_n * own_nodes,
+    )
+    col_parts, row_parts = gather(rounded, (gram,))
     left = call(
         functools.partial(half_form_kernel, runs[1]),
         jax.ShapeDtypeStruct(spread, BF16),

time: 101 us -> 101 us (level)
  local copies, waits for them, and re-layouts: 2.88 us -> 4.75 us
  starting transfers between devices: 57.6 us -> 56.2 us
    unnamed x12 -> x14, local copies, waits for them, and re-layouts: 2.85 us -> 4.71 us
    ppermute x51, starting transfers between devices: 57.6 us -> 56.2 us  [trade(): return lax.ppermute(part, axis, [(i, i ^ d) for i in range(n)])]
    pallas_call x13 -> x14, Pallas kernels: 14.5 us -> 14.2 us  [call(): pl.pallas_call(lambda *refs: kernel(*refs[len(after):]), out_shape=out_sh...]
  transfers between devices with their start and end apart: 51 -> 51, of which waited for: 28 -> 32; matrix products, arithmetic and copies ran while one was open for 0% -> 0% of each run, Pallas kernels for 5% -> 6%
where the time goes in v13:
time: 101 us
  starting transfers between devices  56.2 us (56%)
  waiting for transfers between devices  24.9 us (25%)
  Pallas kernels  14.2 us (14%)
  local copies, waits for them, and re-layouts  4.75 us (5%)
    ppermute x51, starting transfers between devices, trade(): return lax.ppermute(part, axis, [(i, i ^ d) for i in range(n)])  56.2 us
    ppermute x51, waiting for transfers between devices, trade(): return lax.ppermute(part, axis, [(i, i ^ d) for i in range(n)])  24.9 us
    pallas_call x14, Pallas kernels, call(): pl.pallas_call(lambda *refs: kernel(*refs[len(after):]), out_shape=out_sh...  14.2 us
    unnamed x14, local copies, waits for them, and re-layouts  4.71 us
  transfers between devices with their start and end apart: 51, of which 32 were waited for; matrix products, arithmetic and copies ran while one was open for 0% of the time, Pallas kernels for 6%

profile of v13, /device:TPU:0, one launch (start us, length us, event | category | flops | bytes accessed | tf_op | source)
XLA Modules:
  0.0 101.0 jit_solution(13073039186420129812)
XLA Ops:
  0.6 0.9 copy-done.3
  1.6 4.1 %collective-permute-start.8 = (bf16[8,64,128]{2,1,0:T(8,128)(2,1)S(1)}, bf16[8,64,128]{2,1,0:T(8,128)(2,1)S(1)}, u32[]{:S(2)}, u32[]{:S(2)}) collective-permute-start(bf16[8,64,128]{2,1,0:T(8,128)(2,1)S(1)} %shard_map.60.refs_2_.refs_3_), channel_id=1, source_target_pairs={{0,16},{8,24},{16,0},{24,8},{1,17},{9,25},{17,1},{25,9},{2,18},{10... | collective-permute-start | bytes 393224 | tf_op jit(solution)/shard_map/ppermute | solution.py:38
  5.7 2.4 %collective-permute-start.2 = (bf16[8,64,128]{2,1,0:T(8,128)(2,1)S(1)}, bf16[8,64,128]{2,1,0:T(8,128)(2,1)S(1)}, u32[]{:S(2)}, u32[]{:S(2)}) collective-permute-start(bf16[8,64,128]{2,1,0:T(8,128)(2,1)S(1)} %shard_map.60.refs_2_.refs_3_), channel_id=1, source_target_pairs={{0,6},{1,7},{2,4},{3,5},{4,2},{5,3},{6,0},{7,1},{8,14},{9,15},{10,... | collective-permute-start | bytes 393224 | tf_op jit(solution)/shard_map/ppermute | solution.py:38
  9.2 1.6 %collective-permute-start.7 = (bf16[7,64,128]{2,1,0:T(8,128)(2,1)S(1)}, bf16[7,64,128]{2,1,0:T(8,128)(2,1)S(1)}, u32[]{:S(2)}, u32[]{:S(2)}) collective-permute-start(bf16[7,64,128]{2,1,0:T(8,128)(2,1)S(1)} %slice.24), channel_id=1, source_target_pairs={{0,8},{8,0},{16,24},{24,16},{1,9},{9,1},{17,25},{25,17},{2,10},{10... | collective-permute-start | bytes 344072 | tf_op jit(solution)/shard_map/ppermute | solution.py:38
  10.9 1.2 %copy-done = bf16[1,1,32,128,128]{4,3,2,1,0:T(8,128)(2,1)S(1)} copy-done((bf16[1,1,32,128,128]{4,3,2,1,0:T(8,128)(2,1)S(1)}, bf16[1,1,32,128,128]{4,3,2,1,0:T(8,128)(2,1)}, u32[]{:S(2)}) %copy-start) | copy-done | bytes 1048600
  13.5 1.8 %shard_map.59 = (f32[64,128]{1,0:T(8,128)S(1)}, f32[32,128]{1,0:T(8,128)S(1)}, s32[3,32]{1,0:T(4,128)S(1)}) custom-call(s32[3]{0:T(128)S(1)} %pad_add_fusion.refs_0_, s32[32]{0:T(128)S(1)} %bitcast.11, s32[32]{0:T(128)S(1)} %bitcast.12, bf16[32,128,128]{2,1,0:T(8,128)(2,1)S(1)} %bitcast.5), custom_call_target="tpu_custom_call" | custom-call | flops 33554432 | bytes 1048844 | tf_op jit(solution)/shard_map/pallas_call | solution.py:25
  17.9 1.2 %copy-done.1 = bf16[1,1,32,128,128]{4,3,2,1,0:T(8,128)(2,1)S(1)} copy-done((bf16[1,1,32,128,128]{4,3,2,1,0:T(8,128)(2,1)S(1)}, bf16[1,1,32,128,128]{4,3,2,1,0:T(8,128)(2,1)}, u32[]{:S(2)}) %copy-start.1) | copy-done | bytes 1048600
  19.1 1.1 %shard_map.61 = (f32[8,64,128]{2,1,0:T(8,128)S(1)}, bf16[528,128]{1,0:T(8,128)(2,1)S(1)}, bf16[528,128]{1,0:T(8,128)(2,1)S(1)}, bf16[528,128]{1,0:T(8,128)(2,1)S(1)}) custom-call(s32[3,32]{1,0:T(4,128)S(1)} %get-tuple-element.37.refs_0_.refs_1_, bf16[32,128,128]{2,1,0:T(8,128)(2,1)S(1)} %bitcast.6, bf16[8,64,128]{2,1,0:T(8,128)(2,1)S(1)} %shard_map.60.refs_2_.refs_3_, ...), custom_call_target="tpu_custom_call" | custom-call | flops 67108864 | bytes 2113920 | tf_op jit(solution)/shard_map/pallas_call | solution.py:25
  20.6 1.4 %shard_map.62 = (f32[64,64,128]{2,1,0:T(8,128)S(1)}, bf16[4,528,128]{2,1,0:T(8,128)(2,1)S(1)}) custom-call(f32[8,64,128]{2,1,0:T(8,128)S(1)} %get-tuple-element.39.refs_0_.refs_4_, s32[3,32]{1,0:T(4,128)S(1)} %get-tuple-element.37.refs_0_.refs_1_, bf16[32,128,128]{2,1,0:T(8,128)(2,1)S(1)} %bitcast.7, bf16[8,64,128]{2,1,0:T(8,128)(2,1)S(1)} %shard_map.60.refs_2_.refs_3_, ...), custom_call_target="tpu_custom_call" | custom-call | flops 67108864 | bytes 1606016 | tf_op jit(solution)/shard_map/pallas_call | solution.py:25
  22.1 1.6 %collective-permute-start.14 = (bf16[528,128]{1,0:T(8,128)(2,1)S(1)}, bf16[528,128]{1,0:T(8,128)(2,1)S(1)}, u32[]{:S(2)}, u32[]{:S(2)}) collective-permute-start(bf16[528,128]{1,0:T(8,128)(2,1)S(1)} %get-tuple-element.50), channel_id=1, source_target_pairs={{0,8},{8,0},{16,24},{24,16},{1,9},{9,1},{17,25},{25,17},{2,10},{10... | collective-permute-start | bytes 405512 | tf_op jit(solution)/shard_map/ppermute | solution.py:38
  23.7 0.8 collective-permute-start.15
  24.5 2.0 %collective-permute-start.16 = (bf16[528,128]{1,0:T(8,128)(2,1)S(1)}, bf16[528,128]{1,0:T(8,128)(2,1)S(1)}, u32[]{:S(2)}, u32[]{:S(2)}) collective-permute-start(bf16[528,128]{1,0:T(8,128)(2,1)S(1)} %get-tuple-element.52), channel_id=1, source_target_pairs={{0,24},{8,16},{16,8},{24,0},{1,25},{9,17},{17,9},{25,1},{2,26},{10... | collective-permute-start | bytes 405512 | tf_op jit(solution)/shard_map/ppermute | solution.py:38
  26.7 1.6 %collective-permute-start.11 = (bf16[528,128]{1,0:T(8,128)(2,1)S(1)}, bf16[528,128]{1,0:T(8,128)(2,1)S(1)}, u32[]{:S(2)}, u32[]{:S(2)}) collective-permute-start(bf16[528,128]{1,0:T(8,128)(2,1)S(1)} %get-tuple-element.47), channel_id=1, source_target_pairs={{0,2},{1,3},{2,0},{3,1},{4,6},{5,7},{6,4},{7,5},{8,10},{9,11},{10,... | collective-permute-start | bytes 405512 | tf_op jit(solution)/shard_map/ppermute | solution.py:38
  28.2 1.5 %collective-permute-start.12 = (bf16[528,128]{1,0:T(8,128)(2,1)S(1)}, bf16[528,128]{1,0:T(8,128)(2,1)S(1)}, u32[]{:S(2)}, u32[]{:S(2)}) collective-permute-start(bf16[528,128]{1,0:T(8,128)(2,1)S(1)} %get-tuple-element.48), channel_id=1, source_target_pairs={{0,4},{1,5},{2,6},{3,7},{4,0},{5,1},{6,2},{7,3},{8,12},{9,13},{10,... | collective-permute-start | bytes 405512 | tf_op jit(solution)/shard_map/ppermute | solution.py:38
  30.1 2.4 %collective-permute-start.13 = (bf16[528,128]{1,0:T(8,128)(2,1)S(1)}, bf16[528,128]{1,0:T(8,128)(2,1)S(1)}, u32[]{:S(2)}, u32[]{:S(2)}) collective-permute-start(bf16[528,128]{1,0:T(8,128)(2,1)S(1)} %get-tuple-element.49), channel_id=1, source_target_pairs={{0,6},{1,7},{2,4},{3,5},{4,2},{5,3},{6,0},{7,1},{8,14},{9,15},{10,... | collective-permute-start | bytes 405512 | tf_op jit(solution)/shard_map/ppermute | solution.py:38
  32.5 4.3 %collective-permute-done.15.refs_9_ = bf16[528,128]{1,0:T(8,128)(2,1)S(1)} collective-permute-done((bf16[528,128]{1,0:T(8,128)(2,1)S(1)}, bf16[528,128]{1,0:T(8,128)(2,1)S(1)}, u32[]{:S(2)}, u32[]{:S(2)}) %collective-permute-start.15) | collective-permute-done | bytes 135200 | tf_op jit(solution)/shard_map/ppermute | solution.py:38
  37.1 2.8 %collective-permute-start.25 = (bf16[8,64,128]{2,1,0:T(8,128)(2,1)S(1)}, bf16[8,64,128]{2,1,0:T(8,128)(2,1)S(1)}, u32[]{:S(2)}, u32[]{:S(2)}) collective-permute-start(bf16[8,64,128]{2,1,0:T(8,128)(2,1)S(1)} %get-tuple-element.55.refs_2_.refs_3_), channel_id=1, source_target_pairs={{0,16},{8,24},{16,0},{24,8},{1,17},{9,25},{17,1},{25,9},{2,18},{10... | collective-permute-start | bytes 393224 | tf_op jit(solution)/shard_map/ppermute | solution.py:38
  40.0 2.5 %collective-permute-start.19 = (bf16[8,64,128]{2,1,0:T(8,128)(2,1)S(1)}, bf16[8,64,128]{2,1,0:T(8,128)(2,1)S(1)}, u32[]{:S(2)}, u32[]{:S(2)}) collective-permute-start(bf16[8,64,128]{2,1,0:T(8,128)(2,1)S(1)} %get-tuple-element.55.refs_2_.refs_3_), channel_id=1, source_target_pairs={{0,6},{1,7},{2,4},{3,5},{4,2},{5,3},{6,0},{7,1},{8,14},{9,15},{10,... | collective-permute-start | bytes 393224 | tf_op jit(solution)/shard_map/ppermute | solution.py:38
  43.5 2.0 %collective-permute-done.24.refs_5_ = bf16[7,64,128]{2,1,0:T(8,128)(2,1)S(1)} collective-permute-done((bf16[7,64,128]{2,1,0:T(8,128)(2,1)S(1)}, bf16[7,64,128]{2,1,0:T(8,128)(2,1)S(1)}, u32[]{:S(2)}, u32[]{:S(2)}) %collective-permute-start.24) | collective-permute-done | bytes 114720 | tf_op jit(solution)/shard_map/ppermute | solution.py:38
  45.8 1.1 %collective-permute-start.26 = (bf16[9,64,128]{2,1,0:T(8,128)(2,1)S(1)}, bf16[9,64,128]{2,1,0:T(8,128)(2,1)S(1)}, u32[]{:S(2)}, u32[]{:S(2)}) collective-permute-start(bf16[9,64,128]{2,1,0:T(8,128)(2,1)S(1)} %pad_maximum_fusion.1), channel_id=1, source_target_pairs={{0,8},{8,0},{16,24},{24,16},{1,9},{9,1},{17,25},{25,17},{2,10},{10... | collective-permute-start | bytes 442376 | tf_op jit(solution)/shard_map/ppermute | solution.py:38
  48.5 0.8 collective-permute-done.22.refs_8_
  49.5 1.1 %shard_map.65 = (f32[8,64,128]{2,1,0:T(8,128)S(1)}, bf16[512,128]{1,0:T(8,128)(2,1)S(1)}, bf16[512,128]{1,0:T(8,128)(2,1)S(1)}, bf16[512,128]{1,0:T(8,128)(2,1)S(1)}) custom-call(s32[3,32]{1,0:T(4,128)S(1)} %get-tuple-element.37.refs_0_.refs_1_, bf16[32,128,128]{2,1,0:T(8,128)(2,1)S(1)} %bitcast.8, ...), custom_call_target="tpu_custom_call" | custom-call | flops 67108864 | bytes 2097536 | tf_op jit(solution)/shard_map/pallas_call | solution.py:25
  51.0 1.5 %shard_map.66 = (f32[64,64,128]{2,1,0:T(8,128)S(1)}, bf16[4,512,128]{2,1,0:T(8,128)(2,1)S(1)}) custom-call(f32[8,64,128]{2,1,0:T(8,128)S(1)} %get-tuple-element.56.refs_0_.refs_4_, s32[3,32]{1,0:T(4,128)S(1)} %get-tuple-element.37.refs_0_.refs_1_, bf16[32,128,128]{2,1,0:T(8,128)(2,1)S(1)} %bitcast.9, ...), custom_call_target="tpu_custom_call" | custom-call | flops 67108864 | bytes 1573248 | tf_op jit(solution)/shard_map/pallas_call | solution.py:25
  52.5 2.0 %collective-permute-start.31 = (bf16[512,128]{1,0:T(8,128)(2,1)S(1)}, bf16[512,128]{1,0:T(8,128)(2,1)S(1)}, u32[]{:S(2)}, u32[]{:S(2)}) collective-permute-start(bf16[512,128]{1,0:T(8,128)(2,1)S(1)} %get-tuple-element.65), channel_id=1, source_target_pairs={{0,8},{8,0},{16,24},{24,16},{1,9},{9,1},{17,25},{25,17},{2,10},{10... | collective-permute-start | bytes 393224 | tf_op jit(solution)/shard_map/ppermute | solution.py:38
  55.1 1.9 %collective-permute-start.33 = (bf16[512,128]{1,0:T(8,128)(2,1)S(1)}, bf16[512,128]{1,0:T(8,128)(2,1)S(1)}, u32[]{:S(2)}, u32[]{:S(2)}) collective-permute-start(bf16[512,128]{1,0:T(8,128)(2,1)S(1)} %get-tuple-element.67), channel_id=1, source_target_pairs={{0,24},{8,16},{16,8},{24,0},{1,25},{9,17},{17,9},{25,1},{2,26},{10... | collective-permute-start | bytes 393224 | tf_op jit(solution)/shard_map/ppermute | solution.py:38
  57.1 1.5 %collective-permute-start.28 = (bf16[512,128]{1,0:T(8,128)(2,1)S(1)}, bf16[512,128]{1,0:T(8,128)(2,1)S(1)}, u32[]{:S(2)}, u32[]{:S(2)}) collective-permute-start(bf16[512,128]{1,0:T(8,128)(2,1)S(1)} %get-tuple-element.62), channel_id=1, source_target_pairs={{0,2},{1,3},{2,0},{3,1},{4,6},{5,7},{6,4},{7,5},{8,10},{9,11},{10,... | collective-permute-start | bytes 393224 | tf_op jit(solution)/shard_map/ppermute | solution.py:38
  58.7 1.5 %collective-permute-start.29 = (bf16[512,128]{1,0:T(8,128)(2,1)S(1)}, bf16[512,128]{1,0:T(8,128)(2,1)S(1)}, u32[]{:S(2)}, u32[]{:S(2)}) collective-permute-start(bf16[512,128]{1,0:T(8,128)(2,1)S(1)} %get-tuple-element.63), channel_id=1, source_target_pairs={{0,4},{1,5},{2,6},{3,7},{4,0},{5,1},{6,2},{7,3},{8,12},{9,13},{10,... | collective-permute-start | bytes 393224 | tf_op jit(solution)/shard_map/ppermute | solution.py:38
  60.3 2.8 %collective-permute-start.30 = (bf16[512,128]{1,0:T(8,128)(2,1)S(1)}, bf16[512,128]{1,0:T(8,128)(2,1)S(1)}, u32[]{:S(2)}, u32[]{:S(2)}) collective-permute-start(bf16[512,128]{1,0:T(8,128)(2,1)S(1)} %get-tuple-element.64), channel_id=1, source_target_pairs={{0,6},{1,7},{2,4},{3,5},{4,2},{5,3},{6,0},{7,1},{8,14},{9,15},{10,... | collective-permute-start | bytes 393224 | tf_op jit(solution)/shard_map/ppermute | solution.py:38
  63.0 4.4 %collective-permute-done.32.refs_9_ = bf16[512,128]{1,0:T(8,128)(2,1)S(1)} collective-permute-done((bf16[512,128]{1,0:T(8,128)(2,1)S(1)}, bf16[512,128]{1,0:T(8,128)(2,1)S(1)}, u32[]{:S(2)}, u32[]{:S(2)}) %collective-permute-start.32) | collective-permute-done | bytes 131104 | tf_op jit(solution)/shard_map/ppermute | solution.py:38
  67.7 3.0 %collective-permute-start.42 = (bf16[8,64,128]{2,1,0:T(8,128)(2,1)S(1)}, bf16[8,64,128]{2,1,0:T(8,128)(2,1)S(1)}, u32[]{:S(2)}, u32[]{:S(2)}) collective-permute-start(bf16[8,64,128]{2,1,0:T(8,128)(2,1)S(1)} %get-tuple-element.69.refs_2_.refs_3_), channel_id=1, source_target_pairs={{0,16},{8,24},{16,0},{24,8},{1,17},{9,25},{17,1},{25,9},{2,18},{10... | collective-permute-start | bytes 393224 | tf_op jit(solution)/shard_map/ppermute | solution.py:38
  70.7 1.9 %collective-permute-start.36 = (bf16[8,64,128]{2,1,0:T(8,128)(2,1)S(1)}, bf16[8,64,128]{2,1,0:T(8,128)(2,1)S(1)}, u32[]{:S(2)}, u32[]{:S(2)}) collective-permute-start(bf16[8,64,128]{2,1,0:T(8,128)(2,1)S(1)} %get-tuple-element.69.refs_2_.refs_3_), channel_id=1, source_target_pairs={{0,6},{1,7},{2,4},{3,5},{4,2},{5,3},{6,0},{7,1},{8,14},{9,15},{10,... | collective-permute-start | bytes 393224 | tf_op jit(solution)/shard_map/ppermute | solution.py:38
  72.6 0.7 collective-permute-start.35
  73.3 1.0 collective-permute-start.34
  74.9 1.2 %collective-permute-done.41.refs_5_ = bf16[7,64,128]{2,1,0:T(8,128)(2,1)S(1)} collective-permute-done((bf16[7,64,128]{2,1,0:T(8,128)(2,1)S(1)}, bf16[7,64,128]{2,1,0:T(8,128)(2,1)S(1)}, u32[]{:S(2)}, u32[]{:S(2)}) %collective-permute-start.41) | collective-permute-done | bytes 114720 | tf_op jit(solution)/shard_map/ppermute | solution.py:38
  76.3 1.3 %collective-permute-start.43 = (bf16[9,64,128]{2,1,0:T(8,128)(2,1)S(1)}, bf16[9,64,128]{2,1,0:T(8,128)(2,1)S(1)}, u32[]{:S(2)}, u32[]{:S(2)}) collective-permute-start(bf16[9,64,128]{2,1,0:T(8,128)(2,1)S(1)} %pad_maximum_fusion.2), channel_id=1, source_target_pairs={{0,8},{8,0},{16,24},{24,16},{1,9},{9,1},{17,25},{25,17},{2,10},{10... | collective-permute-start | bytes 442376 | tf_op jit(solution)/shard_map/ppermute | solution.py:38
  80.3 1.0 %shard_map.69.refs_1_ = bf16[64,4096]{1,0:T(8,128)(2,1)S(1)} custom-call(s32[3,32]{1,0:T(4,128)S(1)} %get-tuple-element.37.refs_0_.refs_1_, bf16[32,128,128]{2,1,0:T(8,128)(2,1)S(1)} %bitcast.10, bf16[8,64,128]{2,1,0:T(8,128)(2,1)S(1)} %get-tuple-element.69.refs_2_.refs_3_, bf16[8,64,128]{2,1,0:T(8,128)(2,1)S(1)} %collective-permute-done.34.refs_3_, ...), custom_call_target="tpu_custom_call" | custom-call | flops 67108864 | bytes 2097536 | tf_op jit(solution)/shard_map/pallas_call | solution.py:25
  81.5 1.2 %shard_map.71 = f32[40,128]{1,0:T(8,128)S(1)} custom-call(s32[3,32]{1,0:T(4,128)S(1)} %get-tuple-element.37.refs_0_.refs_1_, bf16[64,4096]{1,0:T(8,128)(2,1)S(1)} %shard_map.69.refs_1_, f32[64,128]{1,0:T(8,128)S(1)} %shard_map.70.refs_2_, bf16[8,64,128]{2,1,0:T(8,128)(2,1)S(1)} %get-tuple-element.69.refs_2_.refs_3_, ...), custom_call_target="tpu_custom_call" | custom-call | flops 33554432 | bytes 1081728 | tf_op jit(solution)/shard_map/pallas_call | solution.py:25
  82.9 1.1 %collective-permute-done.44 = f32[40,128]{1,0:T(8,128)S(1)} collective-permute-done((f32[40,128]{1,0:T(8,128)S(1)}, f32[40,128]{1,0:T(8,128)S(1)}, u32[]{:S(2)}, u32[]{:S(2)}) %collective-permute-start.44) | collective-permute-done | bytes 20512 | tf_op jit(solution)/shard_map/ppermute | solution.py:38
  84.0 2.0 %collective-permute-start.47 = (f32[40,128]{1,0:T(8,128)S(1)}, f32[40,128]{1,0:T(8,128)S(1)}, u32[]{:S(2)}, u32[]{:S(2)}) collective-permute-start(f32[40,128]{1,0:T(8,128)S(1)} %add.12), channel_id=1, source_target_pairs={{0,6},{1,7},{2,4},{3,5},{4,2},{5,3},{6,0},{7,1},{8,14},{9,15},{10,... | collective-permute-start | bytes 61448 | tf_op jit(solution)/shard_map/ppermute | solution.py:38
  86.5 0.9 collective-permute-start.45
  87.5 1.3 %collective-permute-done.47 = f32[40,128]{1,0:T(8,128)S(1)} collective-permute-done((f32[40,128]{1,0:T(8,128)S(1)}, f32[40,128]{1,0:T(8,128)S(1)}, u32[]{:S(2)}, u32[]{:S(2)}) %collective-permute-start.47) | collective-permute-done | bytes 20512 | tf_op jit(solution)/shard_map/ppermute | solution.py:38
  88.8 1.0 collective-permute-done.46
  90.3 2.1 %collective-permute-start.50 = (f32[40,128]{1,0:T(8,128)S(1)}, f32[40,128]{1,0:T(8,128)S(1)}, u32[]{:S(2)}, u32[]{:S(2)}) collective-permute-start(f32[40,128]{1,0:T(8,128)S(1)} %add_add_fusion.refs_1_), channel_id=1, source_target_pairs={{0,24},{8,16},{16,8},{24,0},{1,25},{9,17},{17,9},{25,1},{2,26},{10... | collective-permute-start | bytes 61448 | tf_op jit(solution)/shard_map/ppermute | solution.py:38
  92.4 0.9 collective-permute-start.49
  93.3 1.5 %collective-permute-start.48 = (f32[40,128]{1,0:T(8,128)S(1)}, f32[40,128]{1,0:T(8,128)S(1)}, u32[]{:S(2)}, u32[]{:S(2)}) collective-permute-start(f32[40,128]{1,0:T(8,128)S(1)} %add_add_fusion.refs_1_), channel_id=1, source_target_pairs={{0,8},{8,0},{16,24},{24,16},{1,9},{9,1},{17,25},{25,17},{2,10},{10... | collective-permute-start | bytes 61448 | tf_op jit(solution)/shard_map/ppermute | solution.py:38
  94.8 1.2 %collective-permute-done.50.refs_4_ = f32[40,128]{1,0:T(8,128)S(1)} collective-permute-done((f32[40,128]{1,0:T(8,128)S(1)}, f32[40,128]{1,0:T(8,128)S(1)}, u32[]{:S(2)}, u32[]{:S(2)}) %collective-permute-start.50) | collective-permute-done | bytes 20512 | tf_op jit(solution)/shard_map/ppermute | solution.py:38
  96.0 1.2 %collective-permute-done.49.refs_3_ = f32[40,128]{1,0:T(8,128)S(1)} collective-permute-done((f32[40,128]{1,0:T(8,128)S(1)}, f32[40,128]{1,0:T(8,128)S(1)}, u32[]{:S(2)}, u32[]{:S(2)}) %collective-permute-start.49) | collective-permute-done | bytes 20512 | tf_op jit(solution)/shard_map/ppermute | solution.py:38
  97.3 3.8 %shard_map.72 = (f32[64,1024]{1,0:T(8,128)}, f32[64,64]{1,0:T(8,128)}) custom-call(f32[64,1024]{1,0:T(8,128)S(1)} %get-tuple-element.68.refs_0_, f32[40,128]{1,0:T(8,128)S(1)} %add_add_fusion.refs_1_, f32[40,128]{1,0:T(8,128)S(1)} %collective-permute-done.48.refs_2_, f32[40,128]{1,0:T(8,128)S(1)} %collective-permute-done.49.refs_3_, ...), custom_call_target="tpu_custom_call" | custom-call | bytes 344064 | tf_op jit(solution)/shard_map/pallas_call | solution.py:25
  (94 shorter events, 15.8 us)
Async XLA Ops:
  1.6 13.7 %collective-permute-start.8 = (bf16[8,64,128]{2,1,0:T(8,128)(2,1)S(1)}, bf16[8,64,128]{2,1,0:T(8,128)(2,1)S(1)}, u32[]{:S(2)}, u32[]{:S(2)}) collective-permute-start(bf16[8,64,128]{2,1,0:T(8,128)(2,1)S(1)} %shard_map.60.refs_2_.refs_3_), channel_id=1, source_target_pairs={{0,16},{8,24},{16,0},{24,8},{1,17},{9,25},{17,1},{25,9},{2,18},{10... | collective-permute-start | bytes 393224 | tf_op jit(solution)/shard_map/ppermute | solution.py:38
  5.7 10.2 %collective-permute-start.2 = (bf16[8,64,128]{2,1,0:T(8,128)(2,1)S(1)}, bf16[8,64,128]{2,1,0:T(8,128)(2,1)S(1)}, u32[]{:S(2)}, u32[]{:S(2)}) collective-permute-start(bf16[8,64,128]{2,1,0:T(8,128)(2,1)S(1)} %shard_map.60.refs_2_.refs_3_), channel_id=1, source_target_pairs={{0,6},{1,7},{2,4},{3,5},{4,2},{5,3},{6,0},{7,1},{8,14},{9,15},{10,... | collective-permute-start | bytes 393224 | tf_op jit(solution)/shard_map/ppermute | solution.py:38
  8.2 8.2 %collective-permute-start.1 = (bf16[8,64,128]{2,1,0:T(8,128)(2,1)S(1)}, bf16[8,64,128]{2,1,0:T(8,128)(2,1)S(1)}, u32[]{:S(2)}, u32[]{:S(2)}) collective-permute-start(bf16[8,64,128]{2,1,0:T(8,128)(2,1)S(1)} %shard_map.60.refs_2_.refs_3_), channel_id=1, source_target_pairs={{0,4},{1,5},{2,6},{3,7},{4,0},{5,1},{6,2},{7,3},{8,12},{9,13},{10,... | collective-permute-start | bytes 393224 | tf_op jit(solution)/shard_map/ppermute | solution.py:38
  8.7 7.8 %collective-permute-start = (bf16[8,64,128]{2,1,0:T(8,128)(2,1)S(1)}, bf16[8,64,128]{2,1,0:T(8,128)(2,1)S(1)}, u32[]{:S(2)}, u32[]{:S(2)}) collective-permute-start(bf16[8,64,128]{2,1,0:T(8,128)(2,1)S(1)} %shard_map.60.refs_2_.refs_3_), channel_id=1, source_target_pairs={{0,2},{1,3},{2,0},{3,1},{4,6},{5,7},{6,4},{7,5},{8,10},{9,11},{10,... | collective-permute-start | bytes 393224 | tf_op jit(solution)/shard_map/ppermute | solution.py:38
  9.2 6.1 %collective-permute-start.7 = (bf16[7,64,128]{2,1,0:T(8,128)(2,1)S(1)}, bf16[7,64,128]{2,1,0:T(8,128)(2,1)S(1)}, u32[]{:S(2)}, u32[]{:S(2)}) collective-permute-start(bf16[7,64,128]{2,1,0:T(8,128)(2,1)S(1)} %slice.24), channel_id=1, source_target_pairs={{0,8},{8,0},{16,24},{24,16},{1,9},{9,1},{17,25},{25,17},{2,10},{10... | collective-permute-start | bytes 344072 | tf_op jit(solution)/shard_map/ppermute | solution.py:38
  15.3 5.2 %collective-permute-start.9 = (bf16[9,64,128]{2,1,0:T(8,128)(2,1)S(1)}, bf16[9,64,128]{2,1,0:T(8,128)(2,1)S(1)}, u32[]{:S(2)}, u32[]{:S(2)}) collective-permute-start(bf16[9,64,128]{2,1,0:T(8,128)(2,1)S(1)} %pad_maximum_fusion), channel_id=1, source_target_pairs={{0,8},{8,0},{16,24},{24,16},{1,9},{9,1},{17,25},{25,17},{2,10},{10... | collective-permute-start | bytes 442376 | tf_op jit(solution)/shard_map/ppermute | solution.py:38
  15.9 1.3 %collective-permute-start.3 = (bf16[8,64,128]{2,1,0:T(8,128)(2,1)S(1)}, bf16[8,64,128]{2,1,0:T(8,128)(2,1)S(1)}, u32[]{:S(2)}, u32[]{:S(2)}) collective-permute-start(bf16[8,64,128]{2,1,0:T(8,128)(2,1)S(1)} %shard_map.60.refs_2_.refs_3_), channel_id=1, source_target_pairs={{0,1},{1,0},{2,3},{3,2},{4,5},{5,4},{6,7},{7,6},{8,9},{9,8},{10,11... | collective-permute-start | bytes 393224 | tf_op jit(solution)/shard_map/ppermute | solution.py:38
  15.9 1.5 %collective-permute-start.6 = (bf16[8,64,128]{2,1,0:T(8,128)(2,1)S(1)}, bf16[8,64,128]{2,1,0:T(8,128)(2,1)S(1)}, u32[]{:S(2)}, u32[]{:S(2)}) collective-permute-start(bf16[8,64,128]{2,1,0:T(8,128)(2,1)S(1)} %collective-permute-done.2.refs_5_), channel_id=1, source_target_pairs={{0,1},{1,0},{2,3},{3,2},{4,5},{5,4},{6,7},{7,6},{8,9},{9,8},{10,11... | collective-permute-start | bytes 393224 | tf_op jit(solution)/shard_map/ppermute | solution.py:38
  16.4 1.3 %collective-permute-start.5 = (bf16[8,64,128]{2,1,0:T(8,128)(2,1)S(1)}, bf16[8,64,128]{2,1,0:T(8,128)(2,1)S(1)}, u32[]{:S(2)}, u32[]{:S(2)}) collective-permute-start(bf16[8,64,128]{2,1,0:T(8,128)(2,1)S(1)} %collective-permute-done.1.refs_4_), channel_id=1, source_target_pairs={{0,1},{1,0},{2,3},{3,2},{4,5},{5,4},{6,7},{7,6},{8,9},{9,8},{10,11... | collective-permute-start | bytes 393224 | tf_op jit(solution)/shard_map/ppermute | solution.py:38
  16.4 1.5 %collective-permute-start.4 = (bf16[8,64,128]{2,1,0:T(8,128)(2,1)S(1)}, bf16[8,64,128]{2,1,0:T(8,128)(2,1)S(1)}, u32[]{:S(2)}, u32[]{:S(2)}) collective-permute-start(bf16[8,64,128]{2,1,0:T(8,128)(2,1)S(1)} %collective-permute-done.refs_3_), channel_id=1, source_target_pairs={{0,1},{1,0},{2,3},{3,2},{4,5},{5,4},{6,7},{7,6},{8,9},{9,8},{10,11... | collective-permute-start | bytes 393224 | tf_op jit(solution)/shard_map/ppermute | solution.py:38
  22.0 4.5 %collective-permute-start.10 = (bf16[4,528,128]{2,1,0:T(8,128)(2,1)S(1)}, bf16[4,528,128]{2,1,0:T(8,128)(2,1)S(1)}, u32[]{:S(2)}, u32[]{:S(2)}) collective-permute-start(bf16[4,528,128]{2,1,0:T(8,128)(2,1)S(1)} %get-tuple-element.44), channel_id=1, source_target_pairs={{0,1},{1,0},{2,3},{3,2},{4,5},{5,4},{6,7},{7,6},{8,9},{9,8},{10,11... | collective-permute-start | bytes 1622024 | tf_op jit(solution)/shard_map/ppermute | solution.py:38
  22.1 8.0 %collective-permute-start.14 = (bf16[528,128]{1,0:T(8,128)(2,1)S(1)}, bf16[528,128]{1,0:T(8,128)(2,1)S(1)}, u32[]{:S(2)}, u32[]{:S(2)}) collective-permute-start(bf16[528,128]{1,0:T(8,128)(2,1)S(1)} %get-tuple-element.50), channel_id=1, source_target_pairs={{0,8},{8,0},{16,24},{24,16},{1,9},{9,1},{17,25},{25,17},{2,10},{10... | collective-permute-start | bytes 405512 | tf_op jit(solution)/shard_map/ppermute | solution.py:38
  23.7 13.2 %collective-permute-start.15 = (bf16[528,128]{1,0:T(8,128)(2,1)S(1)}, bf16[528,128]{1,0:T(8,128)(2,1)S(1)}, u32[]{:S(2)}, u32[]{:S(2)}) collective-permute-start(bf16[528,128]{1,0:T(8,128)(2,1)S(1)} %get-tuple-element.51), channel_id=1, source_target_pairs={{0,16},{8,24},{16,0},{24,8},{1,17},{9,25},{17,1},{25,9},{2,18},{10... | collective-permute-start | bytes 405512 | tf_op jit(solution)/shard_map/ppermute | solution.py:38
  24.5 12.3 %collective-permute-start.16 = (bf16[528,128]{1,0:T(8,128)(2,1)S(1)}, bf16[528,128]{1,0:T(8,128)(2,1)S(1)}, u32[]{:S(2)}, u32[]{:S(2)}) collective-permute-start(bf16[528,128]{1,0:T(8,128)(2,1)S(1)} %get-tuple-element.52), channel_id=1, source_target_pairs={{0,24},{8,16},{16,8},{24,0},{1,25},{9,17},{17,9},{25,1},{2,26},{10... | collective-permute-start | bytes 405512 | tf_op jit(solution)/shard_map/ppermute | solution.py:38
  26.7 10.2 %collective-permute-start.11 = (bf16[528,128]{1,0:T(8,128)(2,1)S(1)}, bf16[528,128]{1,0:T(8,128)(2,1)S(1)}, u32[]{:S(2)}, u32[]{:S(2)}) collective-permute-start(bf16[528,128]{1,0:T(8,128)(2,1)S(1)} %get-tuple-element.47), channel_id=1, source_target_pairs={{0,2},{1,3},{2,0},{3,1},{4,6},{5,7},{6,4},{7,5},{8,10},{9,11},{10,... | collective-permute-start | bytes 405512 | tf_op jit(solution)/shard_map/ppermute | solution.py:38
  28.2 8.6 %collective-permute-start.12 = (bf16[528,128]{1,0:T(8,128)(2,1)S(1)}, bf16[528,128]{1,0:T(8,128)(2,1)S(1)}, u32[]{:S(2)}, u32[]{:S(2)}) collective-permute-start(bf16[528,128]{1,0:T(8,128)(2,1)S(1)} %get-tuple-element.48), channel_id=1, source_target_pairs={{0,4},{1,5},{2,6},{3,7},{4,0},{5,1},{6,2},{7,3},{8,12},{9,13},{10,... | collective-permute-start | bytes 405512 | tf_op jit(solution)/shard_map/ppermute | solution.py:38
  30.1 6.8 %collective-permute-start.13 = (bf16[528,128]{1,0:T(8,128)(2,1)S(1)}, bf16[528,128]{1,0:T(8,128)(2,1)S(1)}, u32[]{:S(2)}, u32[]{:S(2)}) collective-permute-start(bf16[528,128]{1,0:T(8,128)(2,1)S(1)} %get-tuple-element.49), channel_id=1, source_target_pairs={{0,6},{1,7},{2,4},{3,5},{4,2},{5,3},{6,0},{7,1},{8,14},{9,15},{10,... | collective-permute-start | bytes 405512 | tf_op jit(solution)/shard_map/ppermute | solution.py:38
  37.1 8.7 %collective-permute-start.25 = (bf16[8,64,128]{2,1,0:T(8,128)(2,1)S(1)}, bf16[8,64,128]{2,1,0:T(8,128)(2,1)S(1)}, u32[]{:S(2)}, u32[]{:S(2)}) collective-permute-start(bf16[8,64,128]{2,1,0:T(8,128)(2,1)S(1)} %get-tuple-element.55.refs_2_.refs_3_), channel_id=1, source_target_pairs={{0,16},{8,24},{16,0},{24,8},{1,17},{9,25},{17,1},{25,9},{2,18},{10... | collective-permute-start | bytes 393224 | tf_op jit(solution)/shard_map/ppermute | solution.py:38
  39.9 5.6 %collective-permute-start.24 = (bf16[7,64,128]{2,1,0:T(8,128)(2,1)S(1)}, bf16[7,64,128]{2,1,0:T(8,128)(2,1)S(1)}, u32[]{:S(2)}, u32[]{:S(2)}) collective-permute-start(bf16[7,64,128]{2,1,0:T(8,128)(2,1)S(1)} %slice.20), channel_id=1, source_target_pairs={{0,8},{8,0},{16,24},{24,16},{1,9},{9,1},{17,25},{25,17},{2,10},{10... | collective-permute-start | bytes 344072 | tf_op jit(solution)/shard_map/ppermute | solution.py:38
  40.0 7.1 %collective-permute-start.19 = (bf16[8,64,128]{2,1,0:T(8,128)(2,1)S(1)}, bf16[8,64,128]{2,1,0:T(8,128)(2,1)S(1)}, u32[]{:S(2)}, u32[]{:S(2)}) collective-permute-start(bf16[8,64,128]{2,1,0:T(8,128)(2,1)S(1)} %get-tuple-element.55.refs_2_.refs_3_), channel_id=1, source_target_pairs={{0,6},{1,7},{2,4},{3,5},{4,2},{5,3},{6,0},{7,1},{8,14},{9,15},{10,... | collective-permute-start | bytes 393224 | tf_op jit(solution)/shard_map/ppermute | solution.py:38
  42.5 5.5 %collective-permute-start.18 = (bf16[8,64,128]{2,1,0:T(8,128)(2,1)S(1)}, bf16[8,64,128]{2,1,0:T(8,128)(2,1)S(1)}, u32[]{:S(2)}, u32[]{:S(2)}) collective-permute-start(bf16[8,64,128]{2,1,0:T(8,128)(2,1)S(1)} %get-tuple-element.55.refs_2_.refs_3_), channel_id=1, source_target_pairs={{0,4},{1,5},{2,6},{3,7},{4,0},{5,1},{6,2},{7,3},{8,12},{9,13},{10,... | collective-permute-start | bytes 393224 | tf_op jit(solution)/shard_map/ppermute | solution.py:38
  43.0 5.1 %collective-permute-start.17 = (bf16[8,64,128]{2,1,0:T(8,128)(2,1)S(1)}, bf16[8,64,128]{2,1,0:T(8,128)(2,1)S(1)}, u32[]{:S(2)}, u32[]{:S(2)}) collective-permute-start(bf16[8,64,128]{2,1,0:T(8,128)(2,1)S(1)} %get-tuple-element.55.refs_2_.refs_3_), channel_id=1, source_target_pairs={{0,2},{1,3},{2,0},{3,1},{4,6},{5,7},{6,4},{7,5},{8,10},{9,11},{10,... | collective-permute-start | bytes 393224 | tf_op jit(solution)/shard_map/ppermute | solution.py:38
  45.8 5.2 %collective-permute-start.26 = (bf16[9,64,128]{2,1,0:T(8,128)(2,1)S(1)}, bf16[9,64,128]{2,1,0:T(8,128)(2,1)S(1)}, u32[]{:S(2)}, u32[]{:S(2)}) collective-permute-start(bf16[9,64,128]{2,1,0:T(8,128)(2,1)S(1)} %pad_maximum_fusion.1), channel_id=1, source_target_pairs={{0,8},{8,0},{16,24},{24,16},{1,9},{9,1},{17,25},{25,17},{2,10},{10... | collective-permute-start | bytes 442376 | tf_op jit(solution)/shard_map/ppermute | solution.py:38
  46.9 1.6 %collective-permute-start.20 = (bf16[8,64,128]{2,1,0:T(8,128)(2,1)S(1)}, bf16[8,64,128]{2,1,0:T(8,128)(2,1)S(1)}, u32[]{:S(2)}, u32[]{:S(2)}) collective-permute-start(bf16[8,64,128]{2,1,0:T(8,128)(2,1)S(1)} %get-tuple-element.55.refs_2_.refs_3_), channel_id=1, source_target_pairs={{0,1},{1,0},{2,3},{3,2},{4,5},{5,4},{6,7},{7,6},{8,9},{9,8},{10,11... | collective-permute-start | bytes 393224 | tf_op jit(solution)/shard_map/ppermute | solution.py:38
  47.0 1.4 %collective-permute-start.23 = (bf16[8,64,128]{2,1,0:T(8,128)(2,1)S(1)}, bf16[8,64,128]{2,1,0:T(8,128)(2,1)S(1)}, u32[]{:S(2)}, u32[]{:S(2)}) collective-permute-start(bf16[8,64,128]{2,1,0:T(8,128)(2,1)S(1)} %collective-permute-done.19.refs_5_), channel_id=1, source_target_pairs={{0,1},{1,0},{2,3},{3,2},{4,5},{5,4},{6,7},{7,6},{8,9},{9,8},{10,11... | collective-permute-start | bytes 393224 | tf_op jit(solution)/shard_map/ppermute | solution.py:38
  48.1 1.4 %collective-permute-start.21 = (bf16[8,64,128]{2,1,0:T(8,128)(2,1)S(1)}, bf16[8,64,128]{2,1,0:T(8,128)(2,1)S(1)}, u32[]{:S(2)}, u32[]{:S(2)}) collective-permute-start(bf16[8,64,128]{2,1,0:T(8,128)(2,1)S(1)} %collective-permute-done.17.refs_3_), channel_id=1, source_target_pairs={{0,1},{1,0},{2,3},{3,2},{4,5},{5,4},{6,7},{7,6},{8,9},{9,8},{10,11... | collective-permute-start | bytes 393224 | tf_op jit(solution)/shard_map/ppermute | solution.py:38
  52.5 4.5 %collective-permute-start.27 = (bf16[4,512,128]{2,1,0:T(8,128)(2,1)S(1)}, bf16[4,512,128]{2,1,0:T(8,128)(2,1)S(1)}, u32[]{:S(2)}, u32[]{:S(2)}) collective-permute-start(bf16[4,512,128]{2,1,0:T(8,128)(2,1)S(1)} %get-tuple-element.60), channel_id=1, source_target_pairs={{0,1},{1,0},{2,3},{3,2},{4,5},{5,4},{6,7},{7,6},{8,9},{9,8},{10,11... | collective-permute-start | bytes 1572872 | tf_op jit(solution)/shard_map/ppermute | solution.py:38
  52.5 7.7 %collective-permute-start.31 = (bf16[512,128]{1,0:T(8,128)(2,1)S(1)}, bf16[512,128]{1,0:T(8,128)(2,1)S(1)}, u32[]{:S(2)}, u32[]{:S(2)}) collective-permute-start(bf16[512,128]{1,0:T(8,128)(2,1)S(1)} %get-tuple-element.65), channel_id=1, source_target_pairs={{0,8},{8,0},{16,24},{24,16},{1,9},{9,1},{17,25},{25,17},{2,10},{10... | collective-permute-start | bytes 393224 | tf_op jit(solution)/shard_map/ppermute | solution.py:38
  54.6 12.9 %collective-permute-start.32 = (bf16[512,128]{1,0:T(8,128)(2,1)S(1)}, bf16[512,128]{1,0:T(8,128)(2,1)S(1)}, u32[]{:S(2)}, u32[]{:S(2)}) collective-permute-start(bf16[512,128]{1,0:T(8,128)(2,1)S(1)} %get-tuple-element.66), channel_id=1, source_target_pairs={{0,16},{8,24},{16,0},{24,8},{1,17},{9,25},{17,1},{25,9},{2,18},{10... | collective-permute-start | bytes 393224 | tf_op jit(solution)/shard_map/ppermute | solution.py:38
  55.1 12.3 %collective-permute-start.33 = (bf16[512,128]{1,0:T(8,128)(2,1)S(1)}, bf16[512,128]{1,0:T(8,128)(2,1)S(1)}, u32[]{:S(2)}, u32[]{:S(2)}) collective-permute-start(bf16[512,128]{1,0:T(8,128)(2,1)S(1)} %get-tuple-element.67), channel_id=1, source_target_pairs={{0,24},{8,16},{16,8},{24,0},{1,25},{9,17},{17,9},{25,1},{2,26},{10... | collective-permute-start | bytes 393224 | tf_op jit(solution)/shard_map/ppermute | solution.py:38
  57.1 10.3 %collective-permute-start.28 = (bf16[512,128]{1,0:T(8,128)(2,1)S(1)}, bf16[512,128]{1,0:T(8,128)(2,1)S(1)}, u32[]{:S(2)}, u32[]{:S(2)}) collective-permute-start(bf16[512,128]{1,0:T(8,128)(2,1)S(1)} %get-tuple-element.62), channel_id=1, source_target_pairs={{0,2},{1,3},{2,0},{3,1},{4,6},{5,7},{6,4},{7,5},{8,10},{9,11},{10,... | collective-permute-start | bytes 393224 | tf_op jit(solution)/shard_map/ppermute | solution.py:38
  58.7 8.8 %collective-permute-start.29 = (bf16[512,128]{1,0:T(8,128)(2,1)S(1)}, bf16[512,128]{1,0:T(8,128)(2,1)S(1)}, u32[]{:S(2)}, u32[]{:S(2)}) collective-permute-start(bf16[512,128]{1,0:T(8,128)(2,1)S(1)} %get-tuple-element.63), channel_id=1, source_target_pairs={{0,4},{1,5},{2,6},{3,7},{4,0},{5,1},{6,2},{7,3},{8,12},{9,13},{10,... | collective-permute-start | bytes 393224 | tf_op jit(solution)/shard_map/ppermute | solution.py:38
  60.3 7.2 %collective-permute-start.30 = (bf16[512,128]{1,0:T(8,128)(2,1)S(1)}, bf16[512,128]{1,0:T(8,128)(2,1)S(1)}, u32[]{:S(2)}, u32[]{:S(2)}) collective-permute-start(bf16[512,128]{1,0:T(8,128)(2,1)S(1)} %get-tuple-element.64), channel_id=1, source_target_pairs={{0,6},{1,7},{2,4},{3,5},{4,2},{5,3},{6,0},{7,1},{8,14},{9,15},{10,... | collective-permute-start | bytes 393224 | tf_op jit(solution)/shard_map/ppermute | solution.py:38
  67.7 8.6 %collective-permute-start.42 = (bf16[8,64,128]{2,1,0:T(8,128)(2,1)S(1)}, bf16[8,64,128]{2,1,0:T(8,128)(2,1)S(1)}, u32[]{:S(2)}, u32[]{:S(2)}) collective-permute-start(bf16[8,64,128]{2,1,0:T(8,128)(2,1)S(1)} %get-tuple-element.69.refs_2_.refs_3_), channel_id=1, source_target_pairs={{0,16},{8,24},{16,0},{24,8},{1,17},{9,25},{17,1},{25,9},{2,18},{10... | collective-permute-start | bytes 393224 | tf_op jit(solution)/shard_map/ppermute | solution.py:38
  70.6 5.5 %collective-permute-start.41 = (bf16[7,64,128]{2,1,0:T(8,128)(2,1)S(1)}, bf16[7,64,128]{2,1,0:T(8,128)(2,1)S(1)}, u32[]{:S(2)}, u32[]{:S(2)}) collective-permute-start(bf16[7,64,128]{2,1,0:T(8,128)(2,1)S(1)} %slice.22), channel_id=1, source_target_pairs={{0,8},{8,0},{16,24},{24,16},{1,9},{9,1},{17,25},{25,17},{2,10},{10... | collective-permute-start | bytes 344072 | tf_op jit(solution)/shard_map/ppermute | solution.py:38
  70.7 7.4 %collective-permute-start.36 = (bf16[8,64,128]{2,1,0:T(8,128)(2,1)S(1)}, bf16[8,64,128]{2,1,0:T(8,128)(2,1)S(1)}, u32[]{:S(2)}, u32[]{:S(2)}) collective-permute-start(bf16[8,64,128]{2,1,0:T(8,128)(2,1)S(1)} %get-tuple-element.69.refs_2_.refs_3_), channel_id=1, source_target_pairs={{0,6},{1,7},{2,4},{3,5},{4,2},{5,3},{6,0},{7,1},{8,14},{9,15},{10,... | collective-permute-start | bytes 393224 | tf_op jit(solution)/shard_map/ppermute | solution.py:38
  72.6 6.1 %collective-permute-start.35 = (bf16[8,64,128]{2,1,0:T(8,128)(2,1)S(1)}, bf16[8,64,128]{2,1,0:T(8,128)(2,1)S(1)}, u32[]{:S(2)}, u32[]{:S(2)}) collective-permute-start(bf16[8,64,128]{2,1,0:T(8,128)(2,1)S(1)} %get-tuple-element.69.refs_2_.refs_3_), channel_id=1, source_target_pairs={{0,4},{1,5},{2,6},{3,7},{4,0},{5,1},{6,2},{7,3},{8,12},{9,13},{10,... | collective-permute-start | bytes 393224 | tf_op jit(solution)/shard_map/ppermute | solution.py:38
  73.3 5.4 %collective-permute-start.34 = (bf16[8,64,128]{2,1,0:T(8,128)(2,1)S(1)}, bf16[8,64,128]{2,1,0:T(8,128)(2,1)S(1)}, u32[]{:S(2)}, u32[]{:S(2)}) collective-permute-start(bf16[8,64,128]{2,1,0:T(8,128)(2,1)S(1)} %get-tuple-element.69.refs_2_.refs_3_), channel_id=1, source_target_pairs={{0,2},{1,3},{2,0},{3,1},{4,6},{5,7},{6,4},{7,5},{8,10},{9,11},{10,... | collective-permute-start | bytes 393224 | tf_op jit(solution)/shard_map/ppermute | solution.py:38
  76.3 5.2 %collective-permute-start.43 = (bf16[9,64,128]{2,1,0:T(8,128)(2,1)S(1)}, bf16[9,64,128]{2,1,0:T(8,128)(2,1)S(1)}, u32[]{:S(2)}, u32[]{:S(2)}) collective-permute-start(bf16[9,64,128]{2,1,0:T(8,128)(2,1)S(1)} %pad_maximum_fusion.2), channel_id=1, source_target_pairs={{0,8},{8,0},{16,24},{24,16},{1,9},{9,1},{17,25},{25,17},{2,10},{10... | collective-permute-start | bytes 442376 | tf_op jit(solution)/shard_map/ppermute | solution.py:38
  77.7 1.6 %collective-permute-start.37 = (bf16[8,64,128]{2,1,0:T(8,128)(2,1)S(1)}, bf16[8,64,128]{2,1,0:T(8,128)(2,1)S(1)}, u32[]{:S(2)}, u32[]{:S(2)}) collective-permute-start(bf16[8,64,128]{2,1,0:T(8,128)(2,1)S(1)} %get-tuple-element.69.refs_2_.refs_3_), channel_id=1, source_target_pairs={{0,1},{1,0},{2,3},{3,2},{4,5},{5,4},{6,7},{7,6},{8,9},{9,8},{10,11... | collective-permute-start | bytes 393224 | tf_op jit(solution)/shard_map/ppermute | solution.py:38
  78.1 1.3 %collective-permute-start.40 = (bf16[8,64,128]{2,1,0:T(8,128)(2,1)S(1)}, bf16[8,64,128]{2,1,0:T(8,128)(2,1)S(1)}, u32[]{:S(2)}, u32[]{:S(2)}) collective-permute-start(bf16[8,64,128]{2,1,0:T(8,128)(2,1)S(1)} %collective-permute-done.36.refs_5_), channel_id=1, source_target_pairs={{0,1},{1,0},{2,3},{3,2},{4,5},{5,4},{6,7},{7,6},{8,9},{9,8},{10,11... | collective-permute-start | bytes 393224 | tf_op jit(solution)/shard_map/ppermute | solution.py:38
  78.7 1.5 %collective-permute-start.38 = (bf16[8,64,128]{2,1,0:T(8,128)(2,1)S(1)}, bf16[8,64,128]{2,1,0:T(8,128)(2,1)S(1)}, u32[]{:S(2)}, u32[]{:S(2)}) collective-permute-start(bf16[8,64,128]{2,1,0:T(8,128)(2,1)S(1)} %collective-permute-done.34.refs_3_), channel_id=1, source_target_pairs={{0,1},{1,0},{2,3},{3,2},{4,5},{5,4},{6,7},{7,6},{8,9},{9,8},{10,11... | collective-permute-start | bytes 393224 | tf_op jit(solution)/shard_map/ppermute | solution.py:38
  84.0 4.8 %collective-permute-start.47 = (f32[40,128]{1,0:T(8,128)S(1)}, f32[40,128]{1,0:T(8,128)S(1)}, u32[]{:S(2)}, u32[]{:S(2)}) collective-permute-start(f32[40,128]{1,0:T(8,128)S(1)} %add.12), channel_id=1, source_target_pairs={{0,6},{1,7},{2,4},{3,5},{4,2},{5,3},{6,0},{7,1},{8,14},{9,15},{10,... | collective-permute-start | bytes 61448 | tf_op jit(solution)/shard_map/ppermute | solution.py:38
  85.9 3.8 %collective-permute-start.46 = (f32[40,128]{1,0:T(8,128)S(1)}, f32[40,128]{1,0:T(8,128)S(1)}, u32[]{:S(2)}, u32[]{:S(2)}) collective-permute-start(f32[40,128]{1,0:T(8,128)S(1)} %add.12), channel_id=1, source_target_pairs={{0,4},{1,5},{2,6},{3,7},{4,0},{5,1},{6,2},{7,3},{8,12},{9,13},{10,... | collective-permute-start | bytes 61448 | tf_op jit(solution)/shard_map/ppermute | solution.py:38
  86.5 3.8 %collective-permute-start.45 = (f32[40,128]{1,0:T(8,128)S(1)}, f32[40,128]{1,0:T(8,128)S(1)}, u32[]{:S(2)}, u32[]{:S(2)}) collective-permute-start(f32[40,128]{1,0:T(8,128)S(1)} %add.12), channel_id=1, source_target_pairs={{0,2},{1,3},{2,0},{3,1},{4,6},{5,7},{6,4},{7,5},{8,10},{9,11},{10,... | collective-permute-start | bytes 61448 | tf_op jit(solution)/shard_map/ppermute | solution.py:38
  90.3 5.6 %collective-permute-start.50 = (f32[40,128]{1,0:T(8,128)S(1)}, f32[40,128]{1,0:T(8,128)S(1)}, u32[]{:S(2)}, u32[]{:S(2)}) collective-permute-start(f32[40,128]{1,0:T(8,128)S(1)} %add_add_fusion.refs_1_), channel_id=1, source_target_pairs={{0,24},{8,16},{16,8},{24,0},{1,25},{9,17},{17,9},{25,1},{2,26},{10... | collective-permute-start | bytes 61448 | tf_op jit(solution)/shard_map/ppermute | solution.py:38
  92.4 4.8 %collective-permute-start.49 = (f32[40,128]{1,0:T(8,128)S(1)}, f32[40,128]{1,0:T(8,128)S(1)}, u32[]{:S(2)}, u32[]{:S(2)}) collective-permute-start(f32[40,128]{1,0:T(8,128)S(1)} %add_add_fusion.refs_1_), channel_id=1, source_target_pairs={{0,16},{8,24},{16,0},{24,8},{1,17},{9,25},{17,1},{25,9},{2,18},{10... | collective-permute-start | bytes 61448 | tf_op jit(solution)/shard_map/ppermute | solution.py:38
  93.3 4.0 %collective-permute-start.48 = (f32[40,128]{1,0:T(8,128)S(1)}, f32[40,128]{1,0:T(8,128)S(1)}, u32[]{:S(2)}, u32[]{:S(2)}) collective-permute-start(f32[40,128]{1,0:T(8,128)S(1)} %add_add_fusion.refs_1_), channel_id=1, source_target_pairs={{0,8},{8,0},{16,24},{24,16},{1,9},{9,1},{17,25},{25,17},{2,10},{10... | collective-permute-start | bytes 61448 | tf_op jit(solution)/shard_map/ppermute | solution.py:38
  (10 other events, 47.9 us)

commit v14 on v13

--- a/solution.py
+++ b/solution.py
@@ -70,7 +70,7 @@
             at += count
 
 
-def degree_kernel(group, meta, tile_rows, tile_cols, tiles_ref, row_ref, col_ref, table):
+def degree_kernel(group, meta, tile_rows, tile_cols, tiles_ref, row_ref, col_ref, table, held_ref):
     row_ref[...] = jnp.zeros_like(row_ref)
     col_ref[...] = jnp.zeros_like(col_ref)
     ones = jnp.ones((DEGREE_ROWS, tiles_ref.shape[2]), BF16)
@@ -82,9 +82,11 @@
         table[0, t] = (lax.div(col, group) ^ meta[0]) * group + lax.rem(col, group)
         table[1, t] = apart * group + inside
         table[2, t] = halves * group + inside
-        sums = lax.dot_general(ones, tiles_ref[t], NT, preferred_element_type=F32)
+        tile = tiles_ref[t]
+        held_ref[t] = tile
+        sums = lax.dot_general(ones, tile, NT, preferred_element_type=F32)
         row_ref[pl.ds(table[2, t], 1), :] += sums[:1]
-        col_ref[pl.ds(table[0, t], 1), :] += jnp.sum(tiles_ref[t].astype(F32), 0, keepdims=True)
+        col_ref[pl.ds(table[0, t], 1), :] += jnp.sum(tile.astype(F32), 0, keepdims=True)
 
 
 def column_kernel(runs, degree, table, tiles_ref, *refs):
@@ -410,16 +412,17 @@
 
     rounded = call(round_kernel, rounded_shape, [], 16, [start])
     meta = jnp.stack([lax.axis_index("row"), lax.axis_index("col"), chips_n]).astype(jnp.int32)
-    *degree, table = call(
+    *degree, table, tiles = call(
         functools.partial(degree_kernel, group),
         [jax.ShapeDtypeStruct((n * group, width), F32) for n in (cols_n, rows_n)]
-        + [jax.ShapeDtypeStruct((3, tiles.shape[0]), jnp.int32)],
+        + [jax.ShapeDtypeStruct((3, tiles.shape[0]), jnp.int32)]
+        + [jax.ShapeDtypeStruct(tiles.shape, BF16)],
         [],
         16,
         [meta, tile_rows, tile_cols, tiles],
         4 * tiles.size * DEGREE_ROWS,
         3,
-        outs=[VMEM, VMEM, SMEM],
+        outs=[VMEM, VMEM, SMEM, VMEM],
     )
     first, rounded, degree = call(
         functools.partial(first_kernel, chips_n),

time: 101 us -> 101 us (level)
  local copies, waits for them, and re-layouts: 4.75 us -> 3.52 us
    unnamed x14 -> x10, local copies, waits for them, and re-layouts: 4.71 us -> 3.48 us
  transfers between devices with their start and end apart: 51 -> 51, of which waited for: 32 -> 31; matrix products, arithmetic and copies ran while one was open for 0% -> 0% of each run, Pallas kernels for 6% -> 6%
where the time goes in v14:
time: 101 us; the launch traced here: 100 us
  starting transfers between devices  56.8 us (56%)
  waiting for transfers between devices  24.9 us (25%)
  Pallas kernels  14.1 us (14%)
  local copies, waits for them, and re-layouts  3.52 us (3%)
    ppermute x51, starting transfers between devices, trade(): return lax.ppermute(part, axis, [(i, i ^ d) for i in range(n)])  56.8 us
    ppermute x51, waiting for transfers between devices, trade(): return lax.ppermute(part, axis, [(i, i ^ d) for i in range(n)])  24.9 us
    pallas_call x14, Pallas kernels, call(): pl.pallas_call(lambda *refs: kernel(*refs[len(after):]), out_shape=out_sh...  14.1 us
    unnamed x10, local copies, waits for them, and re-layouts  3.48 us
  transfers between devices with their start and end apart: 51, of which 31 were waited for; matrix products, arithmetic and copies ran while one was open for 0% of the time, Pallas kernels for 6%

profile of v14, /device:TPU:0, one launch (start us, length us, event | category | flops | bytes accessed | tf_op | source)
XLA Modules:
  0.0 100.4 jit_solution(6857286259597621101)
XLA Ops:
  0.6 0.9 copy-done
  1.6 4.1 %collective-permute-start.8 = (bf16[8,64,128]{2,1,0:T(8,128)(2,1)S(1)}, bf16[8,64,128]{2,1,0:T(8,128)(2,1)S(1)}, u32[]{:S(2)}, u32[]{:S(2)}) collective-permute-start(bf16[8,64,128]{2,1,0:T(8,128)(2,1)S(1)} %shard_map.60.refs_2_.refs_3_), channel_id=1, source_target_pairs={{0,16},{8,24},{16,0},{24,8},{1,17},{9,25},{17,1},{25,9},{2,18},{10... | collective-permute-start | bytes 393224 | tf_op jit(solution)/shard_map/ppermute | solution.py:38
  5.7 2.4 %collective-permute-start.2 = (bf16[8,64,128]{2,1,0:T(8,128)(2,1)S(1)}, bf16[8,64,128]{2,1,0:T(8,128)(2,1)S(1)}, u32[]{:S(2)}, u32[]{:S(2)}) collective-permute-start(bf16[8,64,128]{2,1,0:T(8,128)(2,1)S(1)} %shard_map.60.refs_2_.refs_3_), channel_id=1, source_target_pairs={{0,6},{1,7},{2,4},{3,5},{4,2},{5,3},{6,0},{7,1},{8,14},{9,15},{10,... | collective-permute-start | bytes 393224 | tf_op jit(solution)/shard_map/ppermute | solution.py:38
  9.2 1.6 %collective-permute-start.7 = (bf16[7,64,128]{2,1,0:T(8,128)(2,1)S(1)}, bf16[7,64,128]{2,1,0:T(8,128)(2,1)S(1)}, u32[]{:S(2)}, u32[]{:S(2)}) collective-permute-start(bf16[7,64,128]{2,1,0:T(8,128)(2,1)S(1)} %slice.24), channel_id=1, source_target_pairs={{0,8},{8,0},{16,24},{24,16},{1,9},{9,1},{17,25},{25,17},{2,10},{10... | collective-permute-start | bytes 344072 | tf_op jit(solution)/shard_map/ppermute | solution.py:38
  10.9 1.2 %copy-done.2 = bf16[1,1,32,128,128]{4,3,2,1,0:T(8,128)(2,1)S(1)} copy-done((bf16[1,1,32,128,128]{4,3,2,1,0:T(8,128)(2,1)S(1)}, bf16[1,1,32,128,128]{4,3,2,1,0:T(8,128)(2,1)}, u32[]{:S(2)}) %copy-start.2) | copy-done | bytes 1048600
  12.2 0.7 copy-done.3
  13.5 1.7 %shard_map.59 = (f32[64,128]{1,0:T(8,128)S(1)}, f32[32,128]{1,0:T(8,128)S(1)}, s32[3,32]{1,0:T(4,128)S(1)}, bf16[32,128,128]{2,1,0:T(8,128)(2,1)S(1)}) custom-call(s32[3]{0:T(128)S(1)} %pad_add_fusion.refs_0_, s32[32]{0:T(128)S(1)} %bitcast.6, s32[32]{0:T(128)S(1)} %bitcast.7, bf16[32,128,128]{2,1,0:T(8,128)(2,1)S(1)} %bitcast.5), custom_call_target="tpu_custom_call" | custom-call | flops 33554432 | bytes 1048844 | tf_op jit(solution)/shard_map/pallas_call | solution.py:25
  17.8 1.1 %shard_map.61 = (f32[8,64,128]{2,1,0:T(8,128)S(1)}, bf16[528,128]{1,0:T(8,128)(2,1)S(1)}, bf16[528,128]{1,0:T(8,128)(2,1)S(1)}, bf16[528,128]{1,0:T(8,128)(2,1)S(1)}) custom-call(s32[3,32]{1,0:T(4,128)S(1)} %get-tuple-element.38.refs_0_.refs_1_, bf16[32,128,128]{2,1,0:T(8,128)(2,1)S(1)} %get-tuple-element.39.refs_1_.refs_2_, ...), custom_call_target="tpu_custom_call" | custom-call | flops 67108864 | bytes 2113920 | tf_op jit(solution)/shard_map/pallas_call | solution.py:25
  18.9 1.5 %collective-permute-done.9.refs_6_ = bf16[9,64,128]{2,1,0:T(8,128)(2,1)S(1)} collective-permute-done((bf16[9,64,128]{2,1,0:T(8,128)(2,1)S(1)}, bf16[9,64,128]{2,1,0:T(8,128)(2,1)S(1)}, u32[]{:S(2)}, u32[]{:S(2)}) %collective-permute-start.9) | collective-permute-done | bytes 147488 | tf_op jit(solution)/shard_map/ppermute | solution.py:38
  20.5 1.5 %shard_map.62 = (f32[64,64,128]{2,1,0:T(8,128)S(1)}, bf16[4,528,128]{2,1,0:T(8,128)(2,1)S(1)}) custom-call(f32[8,64,128]{2,1,0:T(8,128)S(1)} %get-tuple-element.41.refs_0_.refs_4_, s32[3,32]{1,0:T(4,128)S(1)} %get-tuple-element.38.refs_0_.refs_1_, bf16[32,128,128]{2,1,0:T(8,128)(2,1)S(1)} %get-tuple-element.39.refs_1_.refs_2_, ...), custom_call_target="tpu_custom_call" | custom-call | flops 67108864 | bytes 1606016 | tf_op jit(solution)/shard_map/pallas_call | solution.py:25
  22.5 2.0 %collective-permute-start.15 = (bf16[528,128]{1,0:T(8,128)(2,1)S(1)}, bf16[528,128]{1,0:T(8,128)(2,1)S(1)}, u32[]{:S(2)}, u32[]{:S(2)}) collective-permute-start(bf16[528,128]{1,0:T(8,128)(2,1)S(1)} %get-tuple-element.53), channel_id=1, source_target_pairs={{0,16},{8,24},{16,0},{24,8},{1,17},{9,25},{17,1},{25,9},{2,18},{10... | collective-permute-start | bytes 405512 | tf_op jit(solution)/shard_map/ppermute | solution.py:38
  24.5 1.9 %collective-permute-start.16 = (bf16[528,128]{1,0:T(8,128)(2,1)S(1)}, bf16[528,128]{1,0:T(8,128)(2,1)S(1)}, u32[]{:S(2)}, u32[]{:S(2)}) collective-permute-start(bf16[528,128]{1,0:T(8,128)(2,1)S(1)} %get-tuple-element.54), channel_id=1, source_target_pairs={{0,24},{8,16},{16,8},{24,0},{1,25},{9,17},{17,9},{25,1},{2,26},{10... | collective-permute-start | bytes 405512 | tf_op jit(solution)/shard_map/ppermute | solution.py:38
  26.6 1.6 %collective-permute-start.11 = (bf16[528,128]{1,0:T(8,128)(2,1)S(1)}, bf16[528,128]{1,0:T(8,128)(2,1)S(1)}, u32[]{:S(2)}, u32[]{:S(2)}) collective-permute-start(bf16[528,128]{1,0:T(8,128)(2,1)S(1)} %get-tuple-element.49), channel_id=1, source_target_pairs={{0,2},{1,3},{2,0},{3,1},{4,6},{5,7},{6,4},{7,5},{8,10},{9,11},{10,... | collective-permute-start | bytes 405512 | tf_op jit(solution)/shard_map/ppermute | solution.py:38
  28.1 1.5 %collective-permute-start.12 = (bf16[528,128]{1,0:T(8,128)(2,1)S(1)}, bf16[528,128]{1,0:T(8,128)(2,1)S(1)}, u32[]{:S(2)}, u32[]{:S(2)}) collective-permute-start(bf16[528,128]{1,0:T(8,128)(2,1)S(1)} %get-tuple-element.50), channel_id=1, source_target_pairs={{0,4},{1,5},{2,6},{3,7},{4,0},{5,1},{6,2},{7,3},{8,12},{9,13},{10,... | collective-permute-start | bytes 405512 | tf_op jit(solution)/shard_map/ppermute | solution.py:38
  30.0 2.4 %collective-permute-start.13 = (bf16[528,128]{1,0:T(8,128)(2,1)S(1)}, bf16[528,128]{1,0:T(8,128)(2,1)S(1)}, u32[]{:S(2)}, u32[]{:S(2)}) collective-permute-start(bf16[528,128]{1,0:T(8,128)(2,1)S(1)} %get-tuple-element.51), channel_id=1, source_target_pairs={{0,6},{1,7},{2,4},{3,5},{4,2},{5,3},{6,0},{7,1},{8,14},{9,15},{10,... | collective-permute-start | bytes 405512 | tf_op jit(solution)/shard_map/ppermute | solution.py:38
  32.5 3.2 %collective-permute-done.15.refs_9_ = bf16[528,128]{1,0:T(8,128)(2,1)S(1)} collective-permute-done((bf16[528,128]{1,0:T(8,128)(2,1)S(1)}, bf16[528,128]{1,0:T(8,128)(2,1)S(1)}, u32[]{:S(2)}, u32[]{:S(2)}) %collective-permute-start.15) | collective-permute-done | bytes 135200 | tf_op jit(solution)/shard_map/ppermute | solution.py:38
  36.3 2.6 %collective-permute-start.25 = (bf16[8,64,128]{2,1,0:T(8,128)(2,1)S(1)}, bf16[8,64,128]{2,1,0:T(8,128)(2,1)S(1)}, u32[]{:S(2)}, u32[]{:S(2)}) collective-permute-start(bf16[8,64,128]{2,1,0:T(8,128)(2,1)S(1)} %get-tuple-element.57.refs_2_.refs_3_), channel_id=1, source_target_pairs={{0,16},{8,24},{16,0},{24,8},{1,17},{9,25},{17,1},{25,9},{2,18},{10... | collective-permute-start | bytes 393224 | tf_op jit(solution)/shard_map/ppermute | solution.py:38
  39.1 2.5 %collective-permute-start.19 = (bf16[8,64,128]{2,1,0:T(8,128)(2,1)S(1)}, bf16[8,64,128]{2,1,0:T(8,128)(2,1)S(1)}, u32[]{:S(2)}, u32[]{:S(2)}) collective-permute-start(bf16[8,64,128]{2,1,0:T(8,128)(2,1)S(1)} %get-tuple-element.57.refs_2_.refs_3_), channel_id=1, source_target_pairs={{0,6},{1,7},{2,4},{3,5},{4,2},{5,3},{6,0},{7,1},{8,14},{9,15},{10,... | collective-permute-start | bytes 393224 | tf_op jit(solution)/shard_map/ppermute | solution.py:38
  42.6 2.2 %collective-permute-done.24.refs_5_ = bf16[7,64,128]{2,1,0:T(8,128)(2,1)S(1)} collective-permute-done((bf16[7,64,128]{2,1,0:T(8,128)(2,1)S(1)}, bf16[7,64,128]{2,1,0:T(8,128)(2,1)S(1)}, u32[]{:S(2)}, u32[]{:S(2)}) %collective-permute-start.24) | collective-permute-done | bytes 114720 | tf_op jit(solution)/shard_map/ppermute | solution.py:38
  44.8 1.3 %collective-permute-start.26 = (bf16[9,64,128]{2,1,0:T(8,128)(2,1)S(1)}, bf16[9,64,128]{2,1,0:T(8,128)(2,1)S(1)}, u32[]{:S(2)}, u32[]{:S(2)}) collective-permute-start(bf16[9,64,128]{2,1,0:T(8,128)(2,1)S(1)} %pad_maximum_fusion.1), channel_id=1, source_target_pairs={{0,8},{8,0},{16,24},{24,16},{1,9},{9,1},{17,25},{25,17},{2,10},{10... | collective-permute-start | bytes 442376 | tf_op jit(solution)/shard_map/ppermute | solution.py:38
  47.7 0.8 collective-permute-done.22.refs_8_
  48.7 1.1 %shard_map.65 = (f32[8,64,128]{2,1,0:T(8,128)S(1)}, bf16[512,128]{1,0:T(8,128)(2,1)S(1)}, bf16[512,128]{1,0:T(8,128)(2,1)S(1)}, bf16[512,128]{1,0:T(8,128)(2,1)S(1)}) custom-call(s32[3,32]{1,0:T(4,128)S(1)} %get-tuple-element.38.refs_0_.refs_1_, bf16[32,128,128]{2,1,0:T(8,128)(2,1)S(1)} %get-tuple-element.39.refs_1_.refs_2_, ...), custom_call_target="tpu_custom_call" | custom-call | flops 67108864 | bytes 2097536 | tf_op jit(solution)/shard_map/pallas_call | solution.py:25
  50.0 1.5 %shard_map.66 = (f32[64,64,128]{2,1,0:T(8,128)S(1)}, bf16[4,512,128]{2,1,0:T(8,128)(2,1)S(1)}) custom-call(f32[8,64,128]{2,1,0:T(8,128)S(1)} %get-tuple-element.58.refs_0_.refs_4_, s32[3,32]{1,0:T(4,128)S(1)} %get-tuple-element.38.refs_0_.refs_1_, bf16[32,128,128]{2,1,0:T(8,128)(2,1)S(1)} %get-tuple-element.39.refs_1_.refs_2_, ...), custom_call_target="tpu_custom_call" | custom-call | flops 67108864 | bytes 1573248 | tf_op jit(solution)/shard_map/pallas_call | solution.py:25
  51.7 1.8 %collective-permute-start.31 = (bf16[512,128]{1,0:T(8,128)(2,1)S(1)}, bf16[512,128]{1,0:T(8,128)(2,1)S(1)}, u32[]{:S(2)}, u32[]{:S(2)}) collective-permute-start(bf16[512,128]{1,0:T(8,128)(2,1)S(1)} %get-tuple-element.67), channel_id=1, source_target_pairs={{0,8},{8,0},{16,24},{24,16},{1,9},{9,1},{17,25},{25,17},{2,10},{10... | collective-permute-start | bytes 393224 | tf_op jit(solution)/shard_map/ppermute | solution.py:38
  53.5 1.0 collective-permute-start.32
  54.4 1.6 %collective-permute-start.33 = (bf16[512,128]{1,0:T(8,128)(2,1)S(1)}, bf16[512,128]{1,0:T(8,128)(2,1)S(1)}, u32[]{:S(2)}, u32[]{:S(2)}) collective-permute-start(bf16[512,128]{1,0:T(8,128)(2,1)S(1)} %get-tuple-element.69), channel_id=1, source_target_pairs={{0,24},{8,16},{16,8},{24,0},{1,25},{9,17},{17,9},{25,1},{2,26},{10... | collective-permute-start | bytes 393224 | tf_op jit(solution)/shard_map/ppermute | solution.py:38
  56.2 1.6 %collective-permute-start.28 = (bf16[512,128]{1,0:T(8,128)(2,1)S(1)}, bf16[512,128]{1,0:T(8,128)(2,1)S(1)}, u32[]{:S(2)}, u32[]{:S(2)}) collective-permute-start(bf16[512,128]{1,0:T(8,128)(2,1)S(1)} %get-tuple-element.64), channel_id=1, source_target_pairs={{0,2},{1,3},{2,0},{3,1},{4,6},{5,7},{6,4},{7,5},{8,10},{9,11},{10,... | collective-permute-start | bytes 393224 | tf_op jit(solution)/shard_map/ppermute | solution.py:38
  57.7 1.5 %collective-permute-start.29 = (bf16[512,128]{1,0:T(8,128)(2,1)S(1)}, bf16[512,128]{1,0:T(8,128)(2,1)S(1)}, u32[]{:S(2)}, u32[]{:S(2)}) collective-permute-start(bf16[512,128]{1,0:T(8,128)(2,1)S(1)} %get-tuple-element.65), channel_id=1, source_target_pairs={{0,4},{1,5},{2,6},{3,7},{4,0},{5,1},{6,2},{7,3},{8,12},{9,13},{10,... | collective-permute-start | bytes 393224 | tf_op jit(solution)/shard_map/ppermute | solution.py:38
  59.4 2.8 %collective-permute-start.30 = (bf16[512,128]{1,0:T(8,128)(2,1)S(1)}, bf16[512,128]{1,0:T(8,128)(2,1)S(1)}, u32[]{:S(2)}, u32[]{:S(2)}) collective-permute-start(bf16[512,128]{1,0:T(8,128)(2,1)S(1)} %get-tuple-element.66), channel_id=1, source_target_pairs={{0,6},{1,7},{2,4},{3,5},{4,2},{5,3},{6,0},{7,1},{8,14},{9,15},{10,... | collective-permute-start | bytes 393224 | tf_op jit(solution)/shard_map/ppermute | solution.py:38
  62.2 4.2 %collective-permute-done.32.refs_9_ = bf16[512,128]{1,0:T(8,128)(2,1)S(1)} collective-permute-done((bf16[512,128]{1,0:T(8,128)(2,1)S(1)}, bf16[512,128]{1,0:T(8,128)(2,1)S(1)}, u32[]{:S(2)}, u32[]{:S(2)}) %collective-permute-start.32) | collective-permute-done | bytes 131104 | tf_op jit(solution)/shard_map/ppermute | solution.py:38
  66.6 3.0 %collective-permute-start.42 = (bf16[8,64,128]{2,1,0:T(8,128)(2,1)S(1)}, bf16[8,64,128]{2,1,0:T(8,128)(2,1)S(1)}, u32[]{:S(2)}, u32[]{:S(2)}) collective-permute-start(bf16[8,64,128]{2,1,0:T(8,128)(2,1)S(1)} %get-tuple-element.71.refs_2_.refs_3_), channel_id=1, source_target_pairs={{0,16},{8,24},{16,0},{24,8},{1,17},{9,25},{17,1},{25,9},{2,18},{10... | collective-permute-start | bytes 393224 | tf_op jit(solution)/shard_map/ppermute | solution.py:38
  69.7 2.3 %collective-permute-start.36 = (bf16[8,64,128]{2,1,0:T(8,128)(2,1)S(1)}, bf16[8,64,128]{2,1,0:T(8,128)(2,1)S(1)}, u32[]{:S(2)}, u32[]{:S(2)}) collective-permute-start(bf16[8,64,128]{2,1,0:T(8,128)(2,1)S(1)} %get-tuple-element.71.refs_2_.refs_3_), channel_id=1, source_target_pairs={{0,6},{1,7},{2,4},{3,5},{4,2},{5,3},{6,0},{7,1},{8,14},{9,15},{10,... | collective-permute-start | bytes 393224 | tf_op jit(solution)/shard_map/ppermute | solution.py:38
  72.0 0.7 collective-permute-start.35
  73.9 1.2 %collective-permute-done.41.refs_5_ = bf16[7,64,128]{2,1,0:T(8,128)(2,1)S(1)} collective-permute-done((bf16[7,64,128]{2,1,0:T(8,128)(2,1)S(1)}, bf16[7,64,128]{2,1,0:T(8,128)(2,1)S(1)}, u32[]{:S(2)}, u32[]{:S(2)}) %collective-permute-start.41) | collective-permute-done | bytes 114720 | tf_op jit(solution)/shard_map/ppermute | solution.py:38
  75.2 1.4 %collective-permute-start.43 = (bf16[9,64,128]{2,1,0:T(8,128)(2,1)S(1)}, bf16[9,64,128]{2,1,0:T(8,128)(2,1)S(1)}, u32[]{:S(2)}, u32[]{:S(2)}) collective-permute-start(bf16[9,64,128]{2,1,0:T(8,128)(2,1)S(1)} %pad_maximum_fusion.2), channel_id=1, source_target_pairs={{0,8},{8,0},{16,24},{24,16},{1,9},{9,1},{17,25},{25,17},{2,10},{10... | collective-permute-start | bytes 442376 | tf_op jit(solution)/shard_map/ppermute | solution.py:38
  78.2 0.8 collective-permute-done.39.refs_8_
  79.2 1.0 %shard_map.69.refs_1_ = bf16[64,4096]{1,0:T(8,128)(2,1)S(1)} custom-call(s32[3,32]{1,0:T(4,128)S(1)} %get-tuple-element.38.refs_0_.refs_1_, bf16[32,128,128]{2,1,0:T(8,128)(2,1)S(1)} %get-tuple-element.39.refs_1_.refs_2_, bf16[8,64,128]{2,1,0:T(8,128)(2,1)S(1)} %get-tuple-element.71.refs_2_.refs_3_, bf16[8,64,128]{2,1,0:T(8,128)(2,1)S(1)} %collective-permute-done.34.refs_3_, ...), custom_call_target="tpu_custom_call" | custom-call | flops 67108864 | bytes 2097536 | tf_op jit(solution)/shard_map/pallas_call | solution.py:25
  80.4 1.2 %shard_map.71 = f32[40,128]{1,0:T(8,128)S(1)} custom-call(s32[3,32]{1,0:T(4,128)S(1)} %get-tuple-element.38.refs_0_.refs_1_, bf16[64,4096]{1,0:T(8,128)(2,1)S(1)} %shard_map.69.refs_1_, f32[64,128]{1,0:T(8,128)S(1)} %shard_map.70.refs_2_, bf16[8,64,128]{2,1,0:T(8,128)(2,1)S(1)} %get-tuple-element.71.refs_2_.refs_3_, ...), custom_call_target="tpu_custom_call" | custom-call | flops 33554432 | bytes 1081728 | tf_op jit(solution)/shard_map/pallas_call | solution.py:25
  81.9 1.0 collective-permute-done.44
  82.9 2.5 %collective-permute-start.47 = (f32[40,128]{1,0:T(8,128)S(1)}, f32[40,128]{1,0:T(8,128)S(1)}, u32[]{:S(2)}, u32[]{:S(2)}) collective-permute-start(f32[40,128]{1,0:T(8,128)S(1)} %add.12), channel_id=1, source_target_pairs={{0,6},{1,7},{2,4},{3,5},{4,2},{5,3},{6,0},{7,1},{8,14},{9,15},{10,... | collective-permute-start | bytes 61448 | tf_op jit(solution)/shard_map/ppermute | solution.py:38
  86.4 1.2 %collective-permute-done.47 = f32[40,128]{1,0:T(8,128)S(1)} collective-permute-done((f32[40,128]{1,0:T(8,128)S(1)}, f32[40,128]{1,0:T(8,128)S(1)}, u32[]{:S(2)}, u32[]{:S(2)}) %collective-permute-start.47) | collective-permute-done | bytes 20512 | tf_op jit(solution)/shard_map/ppermute | solution.py:38
  87.6 1.6 %collective-permute-done.46 = f32[40,128]{1,0:T(8,128)S(1)} collective-permute-done((f32[40,128]{1,0:T(8,128)S(1)}, f32[40,128]{1,0:T(8,128)S(1)}, u32[]{:S(2)}, u32[]{:S(2)}) %collective-permute-start.46) | collective-permute-done | bytes 20512 | tf_op jit(solution)/shard_map/ppermute | solution.py:38
  89.6 2.2 %collective-permute-start.50 = (f32[40,128]{1,0:T(8,128)S(1)}, f32[40,128]{1,0:T(8,128)S(1)}, u32[]{:S(2)}, u32[]{:S(2)}) collective-permute-start(f32[40,128]{1,0:T(8,128)S(1)} %add_add_fusion.refs_1_), channel_id=1, source_target_pairs={{0,24},{8,16},{16,8},{24,0},{1,25},{9,17},{17,9},{25,1},{2,26},{10... | collective-permute-start | bytes 61448 | tf_op jit(solution)/shard_map/ppermute | solution.py:38
  91.8 0.9 collective-permute-start.49
  92.7 1.4 %collective-permute-start.48 = (f32[40,128]{1,0:T(8,128)S(1)}, f32[40,128]{1,0:T(8,128)S(1)}, u32[]{:S(2)}, u32[]{:S(2)}) collective-permute-start(f32[40,128]{1,0:T(8,128)S(1)} %add_add_fusion.refs_1_), channel_id=1, source_target_pairs={{0,8},{8,0},{16,24},{24,16},{1,9},{9,1},{17,25},{25,17},{2,10},{10... | collective-permute-start | bytes 61448 | tf_op jit(solution)/shard_map/ppermute | solution.py:38
  94.1 1.2 %collective-permute-done.50.refs_4_ = f32[40,128]{1,0:T(8,128)S(1)} collective-permute-done((f32[40,128]{1,0:T(8,128)S(1)}, f32[40,128]{1,0:T(8,128)S(1)}, u32[]{:S(2)}, u32[]{:S(2)}) %collective-permute-start.50) | collective-permute-done | bytes 20512 | tf_op jit(solution)/shard_map/ppermute | solution.py:38
  95.2 1.3 %collective-permute-done.49.refs_3_ = f32[40,128]{1,0:T(8,128)S(1)} collective-permute-done((f32[40,128]{1,0:T(8,128)S(1)}, f32[40,128]{1,0:T(8,128)S(1)}, u32[]{:S(2)}, u32[]{:S(2)}) %collective-permute-start.49) | collective-permute-done | bytes 20512 | tf_op jit(solution)/shard_map/ppermute | solution.py:38
  96.7 3.8 %shard_map.72 = (f32[64,1024]{1,0:T(8,128)}, f32[64,64]{1,0:T(8,128)}) custom-call(f32[64,1024]{1,0:T(8,128)S(1)} %get-tuple-element.70.refs_0_, f32[40,128]{1,0:T(8,128)S(1)} %add_add_fusion.refs_1_, f32[40,128]{1,0:T(8,128)S(1)} %collective-permute-done.48.refs_2_, f32[40,128]{1,0:T(8,128)S(1)} %collective-permute-done.49.refs_3_, ...), custom_call_target="tpu_custom_call" | custom-call | bytes 344064 | tf_op jit(solution)/shard_map/pallas_call | solution.py:25
  (90 shorter events, 14.8 us)
Async XLA Ops:
  1.6 13.6 %collective-permute-start.8 = (bf16[8,64,128]{2,1,0:T(8,128)(2,1)S(1)}, bf16[8,64,128]{2,1,0:T(8,128)(2,1)S(1)}, u32[]{:S(2)}, u32[]{:S(2)}) collective-permute-start(bf16[8,64,128]{2,1,0:T(8,128)(2,1)S(1)} %shard_map.60.refs_2_.refs_3_), channel_id=1, source_target_pairs={{0,16},{8,24},{16,0},{24,8},{1,17},{9,25},{17,1},{25,9},{2,18},{10... | collective-permute-start | bytes 393224 | tf_op jit(solution)/shard_map/ppermute | solution.py:38
  5.7 10.1 %collective-permute-start.2 = (bf16[8,64,128]{2,1,0:T(8,128)(2,1)S(1)}, bf16[8,64,128]{2,1,0:T(8,128)(2,1)S(1)}, u32[]{:S(2)}, u32[]{:S(2)}) collective-permute-start(bf16[8,64,128]{2,1,0:T(8,128)(2,1)S(1)} %shard_map.60.refs_2_.refs_3_), channel_id=1, source_target_pairs={{0,6},{1,7},{2,4},{3,5},{4,2},{5,3},{6,0},{7,1},{8,14},{9,15},{10,... | collective-permute-start | bytes 393224 | tf_op jit(solution)/shard_map/ppermute | solution.py:38
  8.2 8.1 %collective-permute-start.1 = (bf16[8,64,128]{2,1,0:T(8,128)(2,1)S(1)}, bf16[8,64,128]{2,1,0:T(8,128)(2,1)S(1)}, u32[]{:S(2)}, u32[]{:S(2)}) collective-permute-start(bf16[8,64,128]{2,1,0:T(8,128)(2,1)S(1)} %shard_map.60.refs_2_.refs_3_), channel_id=1, source_target_pairs={{0,4},{1,5},{2,6},{3,7},{4,0},{5,1},{6,2},{7,3},{8,12},{9,13},{10,... | collective-permute-start | bytes 393224 | tf_op jit(solution)/shard_map/ppermute | solution.py:38
  8.7 7.7 %collective-permute-start = (bf16[8,64,128]{2,1,0:T(8,128)(2,1)S(1)}, bf16[8,64,128]{2,1,0:T(8,128)(2,1)S(1)}, u32[]{:S(2)}, u32[]{:S(2)}) collective-permute-start(bf16[8,64,128]{2,1,0:T(8,128)(2,1)S(1)} %shard_map.60.refs_2_.refs_3_), channel_id=1, source_target_pairs={{0,2},{1,3},{2,0},{3,1},{4,6},{5,7},{6,4},{7,5},{8,10},{9,11},{10,... | collective-permute-start | bytes 393224 | tf_op jit(solution)/shard_map/ppermute | solution.py:38
  9.2 6.0 %collective-permute-start.7 = (bf16[7,64,128]{2,1,0:T(8,128)(2,1)S(1)}, bf16[7,64,128]{2,1,0:T(8,128)(2,1)S(1)}, u32[]{:S(2)}, u32[]{:S(2)}) collective-permute-start(bf16[7,64,128]{2,1,0:T(8,128)(2,1)S(1)} %slice.24), channel_id=1, source_target_pairs={{0,8},{8,0},{16,24},{24,16},{1,9},{9,1},{17,25},{25,17},{2,10},{10... | collective-permute-start | bytes 344072 | tf_op jit(solution)/shard_map/ppermute | solution.py:38
  15.3 5.2 %collective-permute-start.9 = (bf16[9,64,128]{2,1,0:T(8,128)(2,1)S(1)}, bf16[9,64,128]{2,1,0:T(8,128)(2,1)S(1)}, u32[]{:S(2)}, u32[]{:S(2)}) collective-permute-start(bf16[9,64,128]{2,1,0:T(8,128)(2,1)S(1)} %pad_maximum_fusion), channel_id=1, source_target_pairs={{0,8},{8,0},{16,24},{24,16},{1,9},{9,1},{17,25},{25,17},{2,10},{10... | collective-permute-start | bytes 442376 | tf_op jit(solution)/shard_map/ppermute | solution.py:38
  15.8 1.3 %collective-permute-start.3 = (bf16[8,64,128]{2,1,0:T(8,128)(2,1)S(1)}, bf16[8,64,128]{2,1,0:T(8,128)(2,1)S(1)}, u32[]{:S(2)}, u32[]{:S(2)}) collective-permute-start(bf16[8,64,128]{2,1,0:T(8,128)(2,1)S(1)} %shard_map.60.refs_2_.refs_3_), channel_id=1, source_target_pairs={{0,1},{1,0},{2,3},{3,2},{4,5},{5,4},{6,7},{7,6},{8,9},{9,8},{10,11... | collective-permute-start | bytes 393224 | tf_op jit(solution)/shard_map/ppermute | solution.py:38
  15.8 1.5 %collective-permute-start.6 = (bf16[8,64,128]{2,1,0:T(8,128)(2,1)S(1)}, bf16[8,64,128]{2,1,0:T(8,128)(2,1)S(1)}, u32[]{:S(2)}, u32[]{:S(2)}) collective-permute-start(bf16[8,64,128]{2,1,0:T(8,128)(2,1)S(1)} %collective-permute-done.2.refs_5_), channel_id=1, source_target_pairs={{0,1},{1,0},{2,3},{3,2},{4,5},{5,4},{6,7},{7,6},{8,9},{9,8},{10,11... | collective-permute-start | bytes 393224 | tf_op jit(solution)/shard_map/ppermute | solution.py:38
  16.3 1.3 %collective-permute-start.5 = (bf16[8,64,128]{2,1,0:T(8,128)(2,1)S(1)}, bf16[8,64,128]{2,1,0:T(8,128)(2,1)S(1)}, u32[]{:S(2)}, u32[]{:S(2)}) collective-permute-start(bf16[8,64,128]{2,1,0:T(8,128)(2,1)S(1)} %collective-permute-done.1.refs_4_), channel_id=1, source_target_pairs={{0,1},{1,0},{2,3},{3,2},{4,5},{5,4},{6,7},{7,6},{8,9},{9,8},{10,11... | collective-permute-start | bytes 393224 | tf_op jit(solution)/shard_map/ppermute | solution.py:38
  16.4 1.5 %collective-permute-start.4 = (bf16[8,64,128]{2,1,0:T(8,128)(2,1)S(1)}, bf16[8,64,128]{2,1,0:T(8,128)(2,1)S(1)}, u32[]{:S(2)}, u32[]{:S(2)}) collective-permute-start(bf16[8,64,128]{2,1,0:T(8,128)(2,1)S(1)} %collective-permute-done.refs_3_), channel_id=1, source_target_pairs={{0,1},{1,0},{2,3},{3,2},{4,5},{5,4},{6,7},{7,6},{8,9},{9,8},{10,11... | collective-permute-start | bytes 393224 | tf_op jit(solution)/shard_map/ppermute | solution.py:38
  21.9 4.5 %collective-permute-start.10 = (bf16[4,528,128]{2,1,0:T(8,128)(2,1)S(1)}, bf16[4,528,128]{2,1,0:T(8,128)(2,1)S(1)}, u32[]{:S(2)}, u32[]{:S(2)}) collective-permute-start(bf16[4,528,128]{2,1,0:T(8,128)(2,1)S(1)} %get-tuple-element.46), channel_id=1, source_target_pairs={{0,1},{1,0},{2,3},{3,2},{4,5},{5,4},{6,7},{7,6},{8,9},{9,8},{10,11... | collective-permute-start | bytes 1622024 | tf_op jit(solution)/shard_map/ppermute | solution.py:38
  22.0 8.0 %collective-permute-start.14 = (bf16[528,128]{1,0:T(8,128)(2,1)S(1)}, bf16[528,128]{1,0:T(8,128)(2,1)S(1)}, u32[]{:S(2)}, u32[]{:S(2)}) collective-permute-start(bf16[528,128]{1,0:T(8,128)(2,1)S(1)} %get-tuple-element.52), channel_id=1, source_target_pairs={{0,8},{8,0},{16,24},{24,16},{1,9},{9,1},{17,25},{25,17},{2,10},{10... | collective-permute-start | bytes 405512 | tf_op jit(solution)/shard_map/ppermute | solution.py:38
  22.5 13.2 %collective-permute-start.15 = (bf16[528,128]{1,0:T(8,128)(2,1)S(1)}, bf16[528,128]{1,0:T(8,128)(2,1)S(1)}, u32[]{:S(2)}, u32[]{:S(2)}) collective-permute-start(bf16[528,128]{1,0:T(8,128)(2,1)S(1)} %get-tuple-element.53), channel_id=1, source_target_pairs={{0,16},{8,24},{16,0},{24,8},{1,17},{9,25},{17,1},{25,9},{2,18},{10... | collective-permute-start | bytes 405512 | tf_op jit(solution)/shard_map/ppermute | solution.py:38
  24.5 11.2 %collective-permute-start.16 = (bf16[528,128]{1,0:T(8,128)(2,1)S(1)}, bf16[528,128]{1,0:T(8,128)(2,1)S(1)}, u32[]{:S(2)}, u32[]{:S(2)}) collective-permute-start(bf16[528,128]{1,0:T(8,128)(2,1)S(1)} %get-tuple-element.54), channel_id=1, source_target_pairs={{0,24},{8,16},{16,8},{24,0},{1,25},{9,17},{17,9},{25,1},{2,26},{10... | collective-permute-start | bytes 405512 | tf_op jit(solution)/shard_map/ppermute | solution.py:38
  26.6 9.1 %collective-permute-start.11 = (bf16[528,128]{1,0:T(8,128)(2,1)S(1)}, bf16[528,128]{1,0:T(8,128)(2,1)S(1)}, u32[]{:S(2)}, u32[]{:S(2)}) collective-permute-start(bf16[528,128]{1,0:T(8,128)(2,1)S(1)} %get-tuple-element.49), channel_id=1, source_target_pairs={{0,2},{1,3},{2,0},{3,1},{4,6},{5,7},{6,4},{7,5},{8,10},{9,11},{10,... | collective-permute-start | bytes 405512 | tf_op jit(solution)/shard_map/ppermute | solution.py:38
  28.1 7.6 %collective-permute-start.12 = (bf16[528,128]{1,0:T(8,128)(2,1)S(1)}, bf16[528,128]{1,0:T(8,128)(2,1)S(1)}, u32[]{:S(2)}, u32[]{:S(2)}) collective-permute-start(bf16[528,128]{1,0:T(8,128)(2,1)S(1)} %get-tuple-element.50), channel_id=1, source_target_pairs={{0,4},{1,5},{2,6},{3,7},{4,0},{5,1},{6,2},{7,3},{8,12},{9,13},{10,... | collective-permute-start | bytes 405512 | tf_op jit(solution)/shard_map/ppermute | solution.py:38
  30.0 6.0 %collective-permute-start.13 = (bf16[528,128]{1,0:T(8,128)(2,1)S(1)}, bf16[528,128]{1,0:T(8,128)(2,1)S(1)}, u32[]{:S(2)}, u32[]{:S(2)}) collective-permute-start(bf16[528,128]{1,0:T(8,128)(2,1)S(1)} %get-tuple-element.51), channel_id=1, source_target_pairs={{0,6},{1,7},{2,4},{3,5},{4,2},{5,3},{6,0},{7,1},{8,14},{9,15},{10,... | collective-permute-start | bytes 405512 | tf_op jit(solution)/shard_map/ppermute | solution.py:38
  36.3 8.6 %collective-permute-start.25 = (bf16[8,64,128]{2,1,0:T(8,128)(2,1)S(1)}, bf16[8,64,128]{2,1,0:T(8,128)(2,1)S(1)}, u32[]{:S(2)}, u32[]{:S(2)}) collective-permute-start(bf16[8,64,128]{2,1,0:T(8,128)(2,1)S(1)} %get-tuple-element.57.refs_2_.refs_3_), channel_id=1, source_target_pairs={{0,16},{8,24},{16,0},{24,8},{1,17},{9,25},{17,1},{25,9},{2,18},{10... | collective-permute-start | bytes 393224 | tf_op jit(solution)/shard_map/ppermute | solution.py:38
  38.9 5.9 %collective-permute-start.24 = (bf16[7,64,128]{2,1,0:T(8,128)(2,1)S(1)}, bf16[7,64,128]{2,1,0:T(8,128)(2,1)S(1)}, u32[]{:S(2)}, u32[]{:S(2)}) collective-permute-start(bf16[7,64,128]{2,1,0:T(8,128)(2,1)S(1)} %slice.20), channel_id=1, source_target_pairs={{0,8},{8,0},{16,24},{24,16},{1,9},{9,1},{17,25},{25,17},{2,10},{10... | collective-permute-start | bytes 344072 | tf_op jit(solution)/shard_map/ppermute | solution.py:38
  39.1 7.1 %collective-permute-start.19 = (bf16[8,64,128]{2,1,0:T(8,128)(2,1)S(1)}, bf16[8,64,128]{2,1,0:T(8,128)(2,1)S(1)}, u32[]{:S(2)}, u32[]{:S(2)}) collective-permute-start(bf16[8,64,128]{2,1,0:T(8,128)(2,1)S(1)} %get-tuple-element.57.refs_2_.refs_3_), channel_id=1, source_target_pairs={{0,6},{1,7},{2,4},{3,5},{4,2},{5,3},{6,0},{7,1},{8,14},{9,15},{10,... | collective-permute-start | bytes 393224 | tf_op jit(solution)/shard_map/ppermute | solution.py:38
  41.5 5.6 %collective-permute-start.18 = (bf16[8,64,128]{2,1,0:T(8,128)(2,1)S(1)}, bf16[8,64,128]{2,1,0:T(8,128)(2,1)S(1)}, u32[]{:S(2)}, u32[]{:S(2)}) collective-permute-start(bf16[8,64,128]{2,1,0:T(8,128)(2,1)S(1)} %get-tuple-element.57.refs_2_.refs_3_), channel_id=1, source_target_pairs={{0,4},{1,5},{2,6},{3,7},{4,0},{5,1},{6,2},{7,3},{8,12},{9,13},{10,... | collective-permute-start | bytes 393224 | tf_op jit(solution)/shard_map/ppermute | solution.py:38
  42.0 5.2 %collective-permute-start.17 = (bf16[8,64,128]{2,1,0:T(8,128)(2,1)S(1)}, bf16[8,64,128]{2,1,0:T(8,128)(2,1)S(1)}, u32[]{:S(2)}, u32[]{:S(2)}) collective-permute-start(bf16[8,64,128]{2,1,0:T(8,128)(2,1)S(1)} %get-tuple-element.57.refs_2_.refs_3_), channel_id=1, source_target_pairs={{0,2},{1,3},{2,0},{3,1},{4,6},{5,7},{6,4},{7,5},{8,10},{9,11},{10,... | collective-permute-start | bytes 393224 | tf_op jit(solution)/shard_map/ppermute | solution.py:38
  44.8 5.2 %collective-permute-start.26 = (bf16[9,64,128]{2,1,0:T(8,128)(2,1)S(1)}, bf16[9,64,128]{2,1,0:T(8,128)(2,1)S(1)}, u32[]{:S(2)}, u32[]{:S(2)}) collective-permute-start(bf16[9,64,128]{2,1,0:T(8,128)(2,1)S(1)} %pad_maximum_fusion.1), channel_id=1, source_target_pairs={{0,8},{8,0},{16,24},{24,16},{1,9},{9,1},{17,25},{25,17},{2,10},{10... | collective-permute-start | bytes 442376 | tf_op jit(solution)/shard_map/ppermute | solution.py:38
  46.1 1.5 %collective-permute-start.20 = (bf16[8,64,128]{2,1,0:T(8,128)(2,1)S(1)}, bf16[8,64,128]{2,1,0:T(8,128)(2,1)S(1)}, u32[]{:S(2)}, u32[]{:S(2)}) collective-permute-start(bf16[8,64,128]{2,1,0:T(8,128)(2,1)S(1)} %get-tuple-element.57.refs_2_.refs_3_), channel_id=1, source_target_pairs={{0,1},{1,0},{2,3},{3,2},{4,5},{5,4},{6,7},{7,6},{8,9},{9,8},{10,11... | collective-permute-start | bytes 393224 | tf_op jit(solution)/shard_map/ppermute | solution.py:38
  46.1 1.5 %collective-permute-start.23 = (bf16[8,64,128]{2,1,0:T(8,128)(2,1)S(1)}, bf16[8,64,128]{2,1,0:T(8,128)(2,1)S(1)}, u32[]{:S(2)}, u32[]{:S(2)}) collective-permute-start(bf16[8,64,128]{2,1,0:T(8,128)(2,1)S(1)} %collective-permute-done.19.refs_5_), channel_id=1, source_target_pairs={{0,1},{1,0},{2,3},{3,2},{4,5},{5,4},{6,7},{7,6},{8,9},{9,8},{10,11... | collective-permute-start | bytes 393224 | tf_op jit(solution)/shard_map/ppermute | solution.py:38
  47.2 1.4 %collective-permute-start.21 = (bf16[8,64,128]{2,1,0:T(8,128)(2,1)S(1)}, bf16[8,64,128]{2,1,0:T(8,128)(2,1)S(1)}, u32[]{:S(2)}, u32[]{:S(2)}) collective-permute-start(bf16[8,64,128]{2,1,0:T(8,128)(2,1)S(1)} %collective-permute-done.17.refs_3_), channel_id=1, source_target_pairs={{0,1},{1,0},{2,3},{3,2},{4,5},{5,4},{6,7},{7,6},{8,9},{9,8},{10,11... | collective-permute-start | bytes 393224 | tf_op jit(solution)/shard_map/ppermute | solution.py:38
  51.5 4.6 %collective-permute-start.27 = (bf16[4,512,128]{2,1,0:T(8,128)(2,1)S(1)}, bf16[4,512,128]{2,1,0:T(8,128)(2,1)S(1)}, u32[]{:S(2)}, u32[]{:S(2)}) collective-permute-start(bf16[4,512,128]{2,1,0:T(8,128)(2,1)S(1)} %get-tuple-element.62), channel_id=1, source_target_pairs={{0,1},{1,0},{2,3},{3,2},{4,5},{5,4},{6,7},{7,6},{8,9},{9,8},{10,11... | collective-permute-start | bytes 1572872 | tf_op jit(solution)/shard_map/ppermute | solution.py:38
  51.7 7.7 %collective-permute-start.31 = (bf16[512,128]{1,0:T(8,128)(2,1)S(1)}, bf16[512,128]{1,0:T(8,128)(2,1)S(1)}, u32[]{:S(2)}, u32[]{:S(2)}) collective-permute-start(bf16[512,128]{1,0:T(8,128)(2,1)S(1)} %get-tuple-element.67), channel_id=1, source_target_pairs={{0,8},{8,0},{16,24},{24,16},{1,9},{9,1},{17,25},{25,17},{2,10},{10... | collective-permute-start | bytes 393224 | tf_op jit(solution)/shard_map/ppermute | solution.py:38
  53.5 12.9 %collective-permute-start.32 = (bf16[512,128]{1,0:T(8,128)(2,1)S(1)}, bf16[512,128]{1,0:T(8,128)(2,1)S(1)}, u32[]{:S(2)}, u32[]{:S(2)}) collective-permute-start(bf16[512,128]{1,0:T(8,128)(2,1)S(1)} %get-tuple-element.68), channel_id=1, source_target_pairs={{0,16},{8,24},{16,0},{24,8},{1,17},{9,25},{17,1},{25,9},{2,18},{10... | collective-permute-start | bytes 393224 | tf_op jit(solution)/shard_map/ppermute | solution.py:38
  54.4 11.9 %collective-permute-start.33 = (bf16[512,128]{1,0:T(8,128)(2,1)S(1)}, bf16[512,128]{1,0:T(8,128)(2,1)S(1)}, u32[]{:S(2)}, u32[]{:S(2)}) collective-permute-start(bf16[512,128]{1,0:T(8,128)(2,1)S(1)} %get-tuple-element.69), channel_id=1, source_target_pairs={{0,24},{8,16},{16,8},{24,0},{1,25},{9,17},{17,9},{25,1},{2,26},{10... | collective-permute-start | bytes 393224 | tf_op jit(solution)/shard_map/ppermute | solution.py:38
  56.2 10.2 %collective-permute-start.28 = (bf16[512,128]{1,0:T(8,128)(2,1)S(1)}, bf16[512,128]{1,0:T(8,128)(2,1)S(1)}, u32[]{:S(2)}, u32[]{:S(2)}) collective-permute-start(bf16[512,128]{1,0:T(8,128)(2,1)S(1)} %get-tuple-element.64), channel_id=1, source_target_pairs={{0,2},{1,3},{2,0},{3,1},{4,6},{5,7},{6,4},{7,5},{8,10},{9,11},{10,... | collective-permute-start | bytes 393224 | tf_op jit(solution)/shard_map/ppermute | solution.py:38
  57.7 8.6 %collective-permute-start.29 = (bf16[512,128]{1,0:T(8,128)(2,1)S(1)}, bf16[512,128]{1,0:T(8,128)(2,1)S(1)}, u32[]{:S(2)}, u32[]{:S(2)}) collective-permute-start(bf16[512,128]{1,0:T(8,128)(2,1)S(1)} %get-tuple-element.65), channel_id=1, source_target_pairs={{0,4},{1,5},{2,6},{3,7},{4,0},{5,1},{6,2},{7,3},{8,12},{9,13},{10,... | collective-permute-start | bytes 393224 | tf_op jit(solution)/shard_map/ppermute | solution.py:38
  59.4 7.0 %collective-permute-start.30 = (bf16[512,128]{1,0:T(8,128)(2,1)S(1)}, bf16[512,128]{1,0:T(8,128)(2,1)S(1)}, u32[]{:S(2)}, u32[]{:S(2)}) collective-permute-start(bf16[512,128]{1,0:T(8,128)(2,1)S(1)} %get-tuple-element.66), channel_id=1, source_target_pairs={{0,6},{1,7},{2,4},{3,5},{4,2},{5,3},{6,0},{7,1},{8,14},{9,15},{10,... | collective-permute-start | bytes 393224 | tf_op jit(solution)/shard_map/ppermute | solution.py:38
  66.6 8.6 %collective-permute-start.42 = (bf16[8,64,128]{2,1,0:T(8,128)(2,1)S(1)}, bf16[8,64,128]{2,1,0:T(8,128)(2,1)S(1)}, u32[]{:S(2)}, u32[]{:S(2)}) collective-permute-start(bf16[8,64,128]{2,1,0:T(8,128)(2,1)S(1)} %get-tuple-element.71.refs_2_.refs_3_), channel_id=1, source_target_pairs={{0,16},{8,24},{16,0},{24,8},{1,17},{9,25},{17,1},{25,9},{2,18},{10... | collective-permute-start | bytes 393224 | tf_op jit(solution)/shard_map/ppermute | solution.py:38
  69.6 5.5 %collective-permute-start.41 = (bf16[7,64,128]{2,1,0:T(8,128)(2,1)S(1)}, bf16[7,64,128]{2,1,0:T(8,128)(2,1)S(1)}, u32[]{:S(2)}, u32[]{:S(2)}) collective-permute-start(bf16[7,64,128]{2,1,0:T(8,128)(2,1)S(1)} %slice.22), channel_id=1, source_target_pairs={{0,8},{8,0},{16,24},{24,16},{1,9},{9,1},{17,25},{25,17},{2,10},{10... | collective-permute-start | bytes 344072 | tf_op jit(solution)/shard_map/ppermute | solution.py:38
  69.7 7.1 %collective-permute-start.36 = (bf16[8,64,128]{2,1,0:T(8,128)(2,1)S(1)}, bf16[8,64,128]{2,1,0:T(8,128)(2,1)S(1)}, u32[]{:S(2)}, u32[]{:S(2)}) collective-permute-start(bf16[8,64,128]{2,1,0:T(8,128)(2,1)S(1)} %get-tuple-element.71.refs_2_.refs_3_), channel_id=1, source_target_pairs={{0,6},{1,7},{2,4},{3,5},{4,2},{5,3},{6,0},{7,1},{8,14},{9,15},{10,... | collective-permute-start | bytes 393224 | tf_op jit(solution)/shard_map/ppermute | solution.py:38
  72.0 5.7 %collective-permute-start.35 = (bf16[8,64,128]{2,1,0:T(8,128)(2,1)S(1)}, bf16[8,64,128]{2,1,0:T(8,128)(2,1)S(1)}, u32[]{:S(2)}, u32[]{:S(2)}) collective-permute-start(bf16[8,64,128]{2,1,0:T(8,128)(2,1)S(1)} %get-tuple-element.71.refs_2_.refs_3_), channel_id=1, source_target_pairs={{0,4},{1,5},{2,6},{3,7},{4,0},{5,1},{6,2},{7,3},{8,12},{9,13},{10,... | collective-permute-start | bytes 393224 | tf_op jit(solution)/shard_map/ppermute | solution.py:38
  72.7 5.1 %collective-permute-start.34 = (bf16[8,64,128]{2,1,0:T(8,128)(2,1)S(1)}, bf16[8,64,128]{2,1,0:T(8,128)(2,1)S(1)}, u32[]{:S(2)}, u32[]{:S(2)}) collective-permute-start(bf16[8,64,128]{2,1,0:T(8,128)(2,1)S(1)} %get-tuple-element.71.refs_2_.refs_3_), channel_id=1, source_target_pairs={{0,2},{1,3},{2,0},{3,1},{4,6},{5,7},{6,4},{7,5},{8,10},{9,11},{10,... | collective-permute-start | bytes 393224 | tf_op jit(solution)/shard_map/ppermute | solution.py:38
  75.2 5.2 %collective-permute-start.43 = (bf16[9,64,128]{2,1,0:T(8,128)(2,1)S(1)}, bf16[9,64,128]{2,1,0:T(8,128)(2,1)S(1)}, u32[]{:S(2)}, u32[]{:S(2)}) collective-permute-start(bf16[9,64,128]{2,1,0:T(8,128)(2,1)S(1)} %pad_maximum_fusion.2), channel_id=1, source_target_pairs={{0,8},{8,0},{16,24},{24,16},{1,9},{9,1},{17,25},{25,17},{2,10},{10... | collective-permute-start | bytes 442376 | tf_op jit(solution)/shard_map/ppermute | solution.py:38
  76.6 1.6 %collective-permute-start.37 = (bf16[8,64,128]{2,1,0:T(8,128)(2,1)S(1)}, bf16[8,64,128]{2,1,0:T(8,128)(2,1)S(1)}, u32[]{:S(2)}, u32[]{:S(2)}) collective-permute-start(bf16[8,64,128]{2,1,0:T(8,128)(2,1)S(1)} %get-tuple-element.71.refs_2_.refs_3_), channel_id=1, source_target_pairs={{0,1},{1,0},{2,3},{3,2},{4,5},{5,4},{6,7},{7,6},{8,9},{9,8},{10,11... | collective-permute-start | bytes 393224 | tf_op jit(solution)/shard_map/ppermute | solution.py:38
  76.8 1.4 %collective-permute-start.40 = (bf16[8,64,128]{2,1,0:T(8,128)(2,1)S(1)}, bf16[8,64,128]{2,1,0:T(8,128)(2,1)S(1)}, u32[]{:S(2)}, u32[]{:S(2)}) collective-permute-start(bf16[8,64,128]{2,1,0:T(8,128)(2,1)S(1)} %collective-permute-done.36.refs_5_), channel_id=1, source_target_pairs={{0,1},{1,0},{2,3},{3,2},{4,5},{5,4},{6,7},{7,6},{8,9},{9,8},{10,11... | collective-permute-start | bytes 393224 | tf_op jit(solution)/shard_map/ppermute | solution.py:38
  77.8 1.5 %collective-permute-start.38 = (bf16[8,64,128]{2,1,0:T(8,128)(2,1)S(1)}, bf16[8,64,128]{2,1,0:T(8,128)(2,1)S(1)}, u32[]{:S(2)}, u32[]{:S(2)}) collective-permute-start(bf16[8,64,128]{2,1,0:T(8,128)(2,1)S(1)} %collective-permute-done.34.refs_3_), channel_id=1, source_target_pairs={{0,1},{1,0},{2,3},{3,2},{4,5},{5,4},{6,7},{7,6},{8,9},{9,8},{10,11... | collective-permute-start | bytes 393224 | tf_op jit(solution)/shard_map/ppermute | solution.py:38
  82.9 4.7 %collective-permute-start.47 = (f32[40,128]{1,0:T(8,128)S(1)}, f32[40,128]{1,0:T(8,128)S(1)}, u32[]{:S(2)}, u32[]{:S(2)}) collective-permute-start(f32[40,128]{1,0:T(8,128)S(1)} %add.12), channel_id=1, source_target_pairs={{0,6},{1,7},{2,4},{3,5},{4,2},{5,3},{6,0},{7,1},{8,14},{9,15},{10,... | collective-permute-start | bytes 61448 | tf_op jit(solution)/shard_map/ppermute | solution.py:38
  85.4 3.8 %collective-permute-start.46 = (f32[40,128]{1,0:T(8,128)S(1)}, f32[40,128]{1,0:T(8,128)S(1)}, u32[]{:S(2)}, u32[]{:S(2)}) collective-permute-start(f32[40,128]{1,0:T(8,128)S(1)} %add.12), channel_id=1, source_target_pairs={{0,4},{1,5},{2,6},{3,7},{4,0},{5,1},{6,2},{7,3},{8,12},{9,13},{10,... | collective-permute-start | bytes 61448 | tf_op jit(solution)/shard_map/ppermute | solution.py:38
  85.8 3.8 %collective-permute-start.45 = (f32[40,128]{1,0:T(8,128)S(1)}, f32[40,128]{1,0:T(8,128)S(1)}, u32[]{:S(2)}, u32[]{:S(2)}) collective-permute-start(f32[40,128]{1,0:T(8,128)S(1)} %add.12), channel_id=1, source_target_pairs={{0,2},{1,3},{2,0},{3,1},{4,6},{5,7},{6,4},{7,5},{8,10},{9,11},{10,... | collective-permute-start | bytes 61448 | tf_op jit(solution)/shard_map/ppermute | solution.py:38
  89.6 5.6 %collective-permute-start.50 = (f32[40,128]{1,0:T(8,128)S(1)}, f32[40,128]{1,0:T(8,128)S(1)}, u32[]{:S(2)}, u32[]{:S(2)}) collective-permute-start(f32[40,128]{1,0:T(8,128)S(1)} %add_add_fusion.refs_1_), channel_id=1, source_target_pairs={{0,24},{8,16},{16,8},{24,0},{1,25},{9,17},{17,9},{25,1},{2,26},{10... | collective-permute-start | bytes 61448 | tf_op jit(solution)/shard_map/ppermute | solution.py:38
  91.8 4.8 %collective-permute-start.49 = (f32[40,128]{1,0:T(8,128)S(1)}, f32[40,128]{1,0:T(8,128)S(1)}, u32[]{:S(2)}, u32[]{:S(2)}) collective-permute-start(f32[40,128]{1,0:T(8,128)S(1)} %add_add_fusion.refs_1_), channel_id=1, source_target_pairs={{0,16},{8,24},{16,0},{24,8},{1,17},{9,25},{17,1},{25,9},{2,18},{10... | collective-permute-start | bytes 61448 | tf_op jit(solution)/shard_map/ppermute | solution.py:38
  92.7 4.0 %collective-permute-start.48 = (f32[40,128]{1,0:T(8,128)S(1)}, f32[40,128]{1,0:T(8,128)S(1)}, u32[]{:S(2)}, u32[]{:S(2)}) collective-permute-start(f32[40,128]{1,0:T(8,128)S(1)} %add_add_fusion.refs_1_), channel_id=1, source_target_pairs={{0,8},{8,0},{16,24},{24,16},{1,9},{9,1},{17,25},{25,17},{2,10},{10... | collective-permute-start | bytes 61448 | tf_op jit(solution)/shard_map/ppermute | solution.py:38
  (8 other events, 23.0 us)

commit v15 on v13

--- a/solution.py
+++ b/solution.py
@@ -20,13 +20,13 @@
 DEGREE_ROWS = 16
 
 
-def call(kernel, out_shape, scratch, limit, args, flops=0, smem=0, after=(), outs=None):
+def call(kernel, out_shape, scratch, limit, args, flops=0, smem=0, after=()):
     moved = sum(x.size * x.dtype.itemsize for x in args)
     return pl.pallas_call(
         lambda *refs: kernel(*refs[len(after) :]),
         out_shape=out_shape,
         in_specs=[ANY] * len(after) + [SMEM] * smem + [VMEM] * (len(args) - smem),
-        out_specs=outs or jax.tree.map(lambda _: VMEM, out_shape),
+        out_specs=jax.tree.map(lambda _: VMEM, out_shape),
         scratch_shapes=scratch,
         compiler_params=pltpu.CompilerParams(vmem_limit_bytes=limit * 2**20),
         cost_estimate=pl.CostEstimate(flops=flops, bytes_accessed=moved, transcendentals=0),
@@ -66,15 +66,12 @@
     for part, places in zip(parts, runs):
         at = 0
         for place, count in places:
-            panel[place : place + count] = part[at : at + count]
+            panel[place : place + count, : part.shape[1], :] = part[at : at + count]
             at += count
 
 
-def degree_kernel(group, meta, tile_rows, tile_cols, tiles_ref, row_ref, col_ref, table):
-    row_ref[...] = jnp.zeros_like(row_ref)
-    col_ref[...] = jnp.zeros_like(col_ref)
-    ones = jnp.ones((DEGREE_ROWS, tiles_ref.shape[2]), BF16)
-    for t in range(tiles_ref.shape[0]):
+def table_kernel(group, meta, tile_rows, tile_cols, table):
+    for t in range(table.shape[1]):
         row, col = tile_rows[t], tile_cols[t]
         apart = lax.div(row, group) ^ meta[1]
         halves = lax.rem(apart, 2) * meta[2] + lax.div(apart, 2)
@@ -82,18 +79,25 @@
         table[0, t] = (lax.div(col, group) ^ meta[0]) * group + lax.rem(col, group)
         table[1, t] = apart * group + inside
         table[2, t] = halves * group + inside
-        sums = lax.dot_general(ones, tiles_ref[t], NT, preferred_element_type=F32)
-        row_ref[pl.ds(table[2, t], 1), :] += sums[:1]
-        col_ref[pl.ds(table[0, t], 1), :] += jnp.sum(tiles_ref[t].astype(F32), 0, keepdims=True)
-
-
-def column_kernel(runs, degree, table, tiles_ref, *refs):
-    parts, refs = refs[: len(runs)], refs[len(runs) :]
-    if degree:
-        sums, *refs = refs
-    own_ref, *send_refs, panel, total = refs
-    group, vectors_n, _ = own_ref.shape
+
+
+def fill_ones(panel, vectors_n):
+    rows = panel.shape[1] - vectors_n
+    if rows:
+        panel[:, vectors_n:, :] = jnp.ones((panel.shape[0], rows, panel.shape[2]), BF16)
+
+
+def degree_of(total, start, group, vectors_n):
+    return jnp.concatenate(
+        [total[start + k, vectors_n : vectors_n + 1, :] for k in range(group)], 0
+    )
+
+
+def column_kernel(runs, table, tiles_ref, *refs):
+    parts, (own_ref, *send_refs, panel, total) = refs[: len(runs)], refs[len(runs) :]
+    group, vectors_n, _ = parts[0].shape
     fill(panel, parts, runs)
+    fill_ones(panel, vectors_n)
     total[...] = jnp.zeros_like(total)
     for t in range(tiles_ref.shape[0]):
         total[table[0, t]] += lax.dot_general(
@@ -101,35 +105,29 @@
         )
     own_ref[...] = total[:group]
     for d, send in enumerate(send_refs, 1):
-        round_sums(send, total, d * group, group)
-        if degree:
-            send[group * vectors_n :, :] = split_degree(sums[d * group : (d + 1) * group, :])
-
-
-def row_kernel(runs, degree, table, tiles_ref, *refs):
-    parts, refs = refs[: len(runs)], refs[len(runs) :]
-    if degree:
-        sums, *refs = refs
-    total, swap_ref, panel = refs
-    half, vectors_n = swap_ref.shape[0], total.shape[1]
-    group = total.shape[0] // (2 * half)
+        round_sums(send, total, d * group, group, vectors_n)
+
+
+def row_kernel(runs, table, tiles_ref, *refs):
+    parts, (total, swap_ref, panel) = refs[: len(runs)], refs[len(runs) :]
+    group, vectors_n, _ = parts[0].shape
+    half = swap_ref.shape[0]
     fill(panel, parts, runs)
+    fill_ones(panel, vectors_n)
     total[...] = jnp.zeros_like(total)
     for t in range(tiles_ref.shape[0]):
         total[table[2, t]] += lax.dot_general(
             panel[table[0, t]], tiles_ref[t], NT, preferred_element_type=F32
         )
     for d in range(half):
-        round_sums(swap_ref.at[d], total, (half + d) * group, group)
-        if degree:
-            rows = slice((half + d) * group, (half + d + 1) * group)
-            swap_ref[d, group * vectors_n :, :] = split_degree(sums[rows, :])
-
-
-def round_sums(send, total, start, group):
-    vectors_n = total.shape[1]
+        round_sums(swap_ref.at[d], total, (half + d) * group, group, vectors_n)
+
+
+def round_sums(send, total, start, group, vectors_n):
     for k in range(group):
-        send[k * vectors_n : (k + 1) * vectors_n, :] = total[start + k].astype(BF16)
+        send[k * vectors_n : (k + 1) * vectors_n, :] = total[start + k, :vectors_n, :].astype(BF16)
+    if total.shape[1] > vectors_n:
+        send[group * vectors_n :, :] = split_degree(degree_of(total, start, group, vectors_n))
 
 
 def products(tiles, table, col_parts, row_parts, runs, degree):
@@ -137,34 +135,31 @@
     half = len(row_parts) // 2
     rows_n = max(place + count for run in runs[0] for place, count in run) // group
     rows = group * vectors_n + (2 * group if degree else 0)
-    own_shape = jax.ShapeDtypeStruct((group, vectors_n, width), F32)
+    height = vectors_n + (DEGREE_ROWS if degree else 0)
     send_shape = jax.ShapeDtypeStruct((rows, width), BF16)
     flops = 2 * tiles.size * vectors_n
 
-    def panels(source, target):
-        return [
-            pltpu.VMEM((source * group, vectors_n, width), BF16),
-            pltpu.VMEM((target * group, vectors_n, width), F32),
-        ]
+    def panel(count):
+        return pltpu.VMEM((count * group, height, width), BF16)
 
     col_own, *col_send = call(
-        functools.partial(column_kernel, runs[1], bool(degree)),
-        [own_shape] + [send_shape] * (rows_n - 1),
-        panels(2 * half, rows_n),
-        24,
-        [table, tiles, *row_parts, *degree[1:]],
+        functools.partial(column_kernel, runs[1]),
+        [jax.ShapeDtypeStruct((group, height, width), F32)] + [send_shape] * (rows_n - 1),
+        [panel(2 * half), pltpu.VMEM((rows_n * group, height, width), F32)],
+        24,
+        [table, tiles, *row_parts],
         flops,
         1,
     )
     kept, swap = call(
-        functools.partial(row_kernel, runs[0], bool(degree)),
+        functools.partial(row_kernel, runs[0]),
         [
-            jax.ShapeDtypeStruct((2 * half * group, vectors_n, width), F32),
+            jax.ShapeDtypeStruct((2 * half * group, height, width), F32),
             jax.ShapeDtypeStruct((half, rows, width), BF16),
         ],
-        panels(rows_n, 2 * half)[:1],
-        24,
-        [table, tiles, *col_parts, *degree[:1]],
+        [panel(rows_n)],
+        24,
+        [table, tiles, *col_parts],
         flops,
         1,
         [col_own],
@@ -172,60 +167,62 @@
     return kept, swap, col_own, col_send
 
 
-def merge_kernel(degree, kept, got, *refs):
+def merge_kernel(degree, vectors_n, kept, got, own_ref, *send_refs):
     if degree:
-        row_degree, own_ref, own_degree, *send_refs = refs
-    else:
-        own_ref, *send_refs = refs
-    group, vectors_n, _ = own_ref.shape
+        own_degree, *send_refs = send_refs
+    group = own_ref.shape[0]
     for k in range(group):
         rows = slice(k * vectors_n, (k + 1) * vectors_n)
-        own_ref[k] = kept[k] + got[0, rows, :].astype(F32)
+        own_ref[k] = kept[k, :vectors_n, :] + got[0, rows, :].astype(F32)
         for d, send in enumerate(send_refs, 1):
-            send[rows, :] = (kept[d * group + k] + got[d, rows, :].astype(F32)).astype(BF16)
+            both = kept[d * group + k, :vectors_n, :] + got[d, rows, :].astype(F32)
+            send[rows, :] = both.astype(BF16)
     if degree:
         for d in range(got.shape[0]):
-            sums = row_degree[d * group : (d + 1) * group, :] + join_degree(got.at[d], group)
+            sums = degree_of(kept, d * group, group, vectors_n) + join_degree(got.at[d], group)
             if d:
                 send_refs[d - 1][group * vectors_n :, :] = split_degree(sums)
             else:
                 own_degree[...] = sums
 
 
-def merge(kept, got, degree):
-    half, (_, vectors_n, width) = got.shape[0], kept.shape
+def merge(kept, got, vectors_n, degree):
+    half, width = got.shape[0], got.shape[2]
     group = kept.shape[0] // (2 * half)
     out_shape = [jax.ShapeDtypeStruct((group, vectors_n, width), F32)]
     if degree:
         out_shape += [jax.ShapeDtypeStruct((group, width), F32)]
     out_shape += [jax.ShapeDtypeStruct(got.shape[1:], BF16)] * (half - 1)
-    kernel = functools.partial(merge_kernel, bool(degree))
-    return call(kernel, out_shape, [], 24, [kept, got, *degree[:1]])
-
-
-def gathered_sum(own, received, k):
-    total = own[k]
-    rows = slice(k * total.shape[0], (k + 1) * total.shape[0])
+    kernel = functools.partial(merge_kernel, degree, vectors_n)
+    return call(kernel, out_shape, [], 24, [kept, got])
+
+
+def gathered_sum(own, received, k, vectors_n):
+    total = own[k, :vectors_n, :]
+    rows = slice(k * vectors_n, (k + 1) * vectors_n)
     for part in received:
         total = total + part[rows, :].astype(F32)
     return total
 
 
-def symmetric_part(row_own, row_refs, col_own, col_refs, k):
-    return 0.5 * (gathered_sum(row_own, row_refs, k) + gathered_sum(col_own, col_refs, k))
-
-
-def first_kernel(chips_n, vec_ref, row_degree, col_degree, row_own, col_own, *refs):
+def symmetric_part(row_own, row_refs, col_own, col_refs, k, vectors_n):
+    return 0.5 * (
+        gathered_sum(row_own, row_refs, k, vectors_n)
+        + gathered_sum(col_own, col_refs, k, vectors_n)
+    )
+
+
+def first_kernel(chips_n, vec_ref, row_degree, row_own, col_own, *refs):
     row_refs, refs = refs[: chips_n - 1], refs[chips_n - 1 :]
     col_refs, (first_ref, rounded_ref, degree_ref) = refs[:-3], refs[-3:]
-    group, _, width = rounded_ref.shape
-    degree = row_degree[...] + col_degree[:group, :]
+    group, vectors_n, width = rounded_ref.shape
+    degree = row_degree[...] + degree_of(col_own, 0, group, vectors_n)
     for part in (*row_refs, *col_refs):
         degree += join_degree(part, group)
     degree = 0.5 * degree
     degree_ref[...] = degree
     for k, vec in enumerate(tiles_first(vec_ref, width)):
-        symmetric = symmetric_part(row_own, row_refs, col_own, col_refs, k)
+        symmetric = symmetric_part(row_own, row_refs, col_own, col_refs, k, vectors_n)
         image = degree[k : k + 1, :] * vec - symmetric
         first = (image - CENTER * vec) / HALF_WIDTH
         first_ref[:, k * width : (k + 1) * width] = first
@@ -235,9 +232,9 @@
 def filter_kernel(chips_n, start_ref, first_ref, degree_ref, row_own, col_own, *refs):
     row_refs, refs = refs[: chips_n - 1], refs[chips_n - 1 :]
     col_refs, (filtered_ref, rounded_ref) = refs[:-2], refs[-2:]
-    width = rounded_ref.shape[2]
+    _, vectors_n, width = rounded_ref.shape
     for k, vec in enumerate(tiles_first(first_ref, width)):
-        symmetric = symmetric_part(row_own, row_refs, col_own, col_refs, k)
+        symmetric = symmetric_part(row_own, row_refs, col_own, col_refs, k, vectors_n)
         columns = slice(k * width, (k + 1) * width)
         image = degree_ref[k : k + 1, :] * vec - symmetric
         filtered = 2.0 * (image - CENTER * vec) / HALF_WIDTH - start_ref[:, columns]
@@ -398,42 +395,37 @@
         chips = [rounded, *exchange([rounded] * (chips_n - 1), "col", 2)]
         return held, chips + [trade(chip, "col", 1) for chip in chips]
 
-    def apply(rounded, degree=()):
-        kept, swap, col_own, col_send = products(tiles, table, *gather(rounded, degree), runs, degree)
+    def apply(rounded, table, degree, first=()):
+        kept, swap, col_own, col_send = products(
+            tiles, table, *gather(rounded, first), runs, degree
+        )
         col_got = exchange(col_send, "row")
-        row_own, *row_send = merge(kept, trade(swap, "col", 1), degree)
-        if degree:
-            own_degree, *row_send = row_send
-        row_got = exchange(row_send, "col", 2)
-        sums = [row_own, col_own, *row_got, *col_got]
-        return [own_degree, degree[1], *sums] if degree else sums
+        row_own, *row_send = merge(kept, trade(swap, "col", 1), vectors_n, degree)
+        row_degree = row_send[:1] if degree else []
+        row_got = exchange(row_send[len(row_degree) :], "col", 2)
+        return [*row_degree, row_own, col_own, *row_got, *col_got]
 
     rounded = call(round_kernel, rounded_shape, [], 16, [start])
     meta = jnp.stack([lax.axis_index("row"), lax.axis_index("col"), chips_n]).astype(jnp.int32)
-    *degree, table = call(
-        functools.partial(degree_kernel, group),
-        [jax.ShapeDtypeStruct((n * group, width), F32) for n in (cols_n, rows_n)]
-        + [jax.ShapeDtypeStruct((3, tiles.shape[0]), jnp.int32)],
-        [],
-        16,
-        [meta, tile_rows, tile_cols, tiles],
-        4 * tiles.size * DEGREE_ROWS,
-        3,
-        outs=[VMEM, VMEM, SMEM],
-    )
+    table = pl.pallas_call(
+        functools.partial(table_kernel, group),
+        out_shape=jax.ShapeDtypeStruct((3, tiles.shape[0]), jnp.int32),
+        in_specs=[SMEM] * 3,
+        out_specs=SMEM,
+    )(meta, tile_rows, tile_cols)
     first, rounded, degree = call(
         functools.partial(first_kernel, chips_n),
         [vector_shape, rounded_shape, degree_shape],
         [],
         24,
-        [start, *apply(rounded, tuple(degree))],
+        [start, *apply(rounded, table, True, (table,))],
     )
     filtered, rounded = call(
         functools.partial(filter_kernel, chips_n),
         [vector_shape, rounded_shape],
         [],
         24,
-        [start, first, degree, *apply(rounded)],
+        [start, first, degree, *apply(rounded, table, False)],
     )
     gram = call(
         gram_kernel,

time: 101 us -> 101 us (level)
  waiting for transfers between devices: 24.9 us -> 27.4 us
  starting transfers between devices: 56.2 us -> 54 us
  local copies, waits for them, and re-layouts: 4.75 us -> 2.89 us
    ppermute x51, waiting for transfers between devices: 24.9 us -> 27.4 us  [trade(): return lax.ppermute(part, axis, [(i, i ^ d) for i in range(n)])]
    ppermute x51, starting transfers between devices: 56.2 us -> 54 us  [trade(): return lax.ppermute(part, axis, [(i, i ^ d) for i in range(n)])]
    unnamed x14 -> x10, local copies, waits for them, and re-layouts: 4.71 us -> 2.86 us
    pallas_call x0 -> x1, Pallas kernels: none -> 1.62 us  [local(): pl.pallas_call(functools.partial(table_kernel, group), out_shape=jax.Shap...]
    pallas_call x14 -> x13, Pallas kernels: 14.2 us -> 12.8 us  [call(): pl.pallas_call(lambda *refs: kernel(*refs[len(after):]), out_shape=out_sh...]
  transfers between devices with their start and end apart: 51 -> 51, of which waited for: 32 -> 30; matrix products, arithmetic and copies ran while one was open for 0% -> 1% of each run, Pallas kernels for 6% -> 6%
where the time goes in v15:
time: 101 us; the launch traced here: 100 us
  starting transfers between devices  54 us (53%)
  waiting for transfers between devices  27.4 us (27%)
  Pallas kernels  14.4 us (14%)
  local copies, waits for them, and re-layouts  2.89 us (3%)
    ppermute x51, starting transfers between devices, trade(): return lax.ppermute(part, axis, [(i, i ^ d) for i in range(n)])  54 us
    ppermute x51, waiting for transfers between devices, trade(): return lax.ppermute(part, axis, [(i, i ^ d) for i in range(n)])  27.4 us
    pallas_call x13, Pallas kernels, call(): pl.pallas_call(lambda *refs: kernel(*refs[len(after):]), out_shape=out_sh...  12.8 us
    unnamed x10, local copies, waits for them, and re-layouts  2.86 us
  transfers between devices with their start and end apart: 51, of which 30 were waited for; matrix products, arithmetic and copies ran while one was open for 1% of the time, Pallas kernels for 6%

profile of v15, /device:TPU:0, one launch (start us, length us, event | category | flops | bytes accessed | tf_op | source)
XLA Modules:
  0.0 100.4 jit_solution(16658894825587287855)
XLA Ops:
  0.6 0.9 copy-done.2
  1.6 4.1 %collective-permute-start.8 = (bf16[8,64,128]{2,1,0:T(8,128)(2,1)S(1)}, bf16[8,64,128]{2,1,0:T(8,128)(2,1)S(1)}, u32[]{:S(2)}, u32[]{:S(2)}) collective-permute-start(bf16[8,64,128]{2,1,0:T(8,128)(2,1)S(1)} %shard_map.60.refs_2_.refs_3_), channel_id=1, source_target_pairs={{0,16},{8,24},{16,0},{24,8},{1,17},{9,25},{17,1},{25,9},{2,18},{10... | collective-permute-start | bytes 393224 | tf_op jit(solution)/shard_map/ppermute | solution.py:38
  5.7 1.6 %collective-permute-start.7 = (bf16[7,64,128]{2,1,0:T(8,128)(2,1)S(1)}, bf16[7,64,128]{2,1,0:T(8,128)(2,1)S(1)}, u32[]{:S(2)}, u32[]{:S(2)}) collective-permute-start(bf16[7,64,128]{2,1,0:T(8,128)(2,1)S(1)} %slice.24), channel_id=1, source_target_pairs={{0,8},{8,0},{16,24},{24,16},{1,9},{9,1},{17,25},{25,17},{2,10},{10... | collective-permute-start | bytes 344072 | tf_op jit(solution)/shard_map/ppermute | solution.py:38
  7.4 2.4 %collective-permute-start.2 = (bf16[8,64,128]{2,1,0:T(8,128)(2,1)S(1)}, bf16[8,64,128]{2,1,0:T(8,128)(2,1)S(1)}, u32[]{:S(2)}, u32[]{:S(2)}) collective-permute-start(bf16[8,64,128]{2,1,0:T(8,128)(2,1)S(1)} %shard_map.60.refs_2_.refs_3_), channel_id=1, source_target_pairs={{0,6},{1,7},{2,4},{3,5},{4,2},{5,3},{6,0},{7,1},{8,14},{9,15},{10,... | collective-permute-start | bytes 393224 | tf_op jit(solution)/shard_map/ppermute | solution.py:38
  11.5 1.6 %shard_map.59.refs_0_.refs_1_ = s32[3,32]{1,0:T(4,128)} custom-call(s32[3]{0:T(128)} %pad_add_fusion.meta, s32[32]{0:T(128)} %bitcast.10, s32[32]{0:T(128)} %bitcast.11), custom_call_target="tpu_custom_call" | custom-call | tf_op jit(solution)/shard_map/pallas_call | solution.py:410
  14.2 1.5 %collective-permute-done.1.refs_4_ = bf16[8,64,128]{2,1,0:T(8,128)(2,1)S(1)} collective-permute-done((bf16[8,64,128]{2,1,0:T(8,128)(2,1)S(1)}, bf16[8,64,128]{2,1,0:T(8,128)(2,1)S(1)}, u32[]{:S(2)}, u32[]{:S(2)}) %collective-permute-start.1) | collective-permute-done | bytes 131104 | tf_op jit(solution)/shard_map/ppermute | solution.py:38
  16.3 0.8 collective-permute-done.5.refs_8_
  17.3 1.2 %copy-done = bf16[1,1,32,128,128]{4,3,2,1,0:T(8,128)(2,1)S(1)} copy-done((bf16[1,1,32,128,128]{4,3,2,1,0:T(8,128)(2,1)S(1)}, bf16[1,1,32,128,128]{4,3,2,1,0:T(8,128)(2,1)}, u32[]{:S(2)}) %copy-start) | copy-done | bytes 1048600
  19.2 1.3 %shard_map.61 = (f32[8,80,128]{2,1,0:T(8,128)S(1)}, bf16[528,128]{1,0:T(8,128)(2,1)S(1)}, bf16[528,128]{1,0:T(8,128)(2,1)S(1)}, bf16[528,128]{1,0:T(8,128)(2,1)S(1)}) custom-call(s32[3,32]{1,0:T(4,128)S(1)} %copy-done.4, bf16[32,128,128]{2,1,0:T(8,128)(2,1)S(1)} %bitcast.5, bf16[8,64,128]{2,1,0:T(8,128)(2,1)S(1)} %shard_map.60.refs_2_.refs_3_, ...), custom_call_target="tpu_custom_call" | custom-call | flops 67108864 | bytes 2097536 | tf_op jit(solution)/shard_map/pallas_call | solution.py:25
  20.5 1.7 %shard_map.62 = (f32[64,80,128]{2,1,0:T(8,128)S(1)}, bf16[4,528,128]{2,1,0:T(8,128)(2,1)S(1)}) custom-call(f32[8,80,128]{2,1,0:T(8,128)S(1)} %get-tuple-element.34.refs_0_.refs_3_, s32[3,32]{1,0:T(4,128)S(1)} %copy-done.4, bf16[32,128,128]{2,1,0:T(8,128)(2,1)S(1)} %bitcast.6, bf16[8,64,128]{2,1,0:T(8,128)(2,1)S(1)} %shard_map.60.refs_2_.refs_3_, ...), custom_call_target="tpu_custom_call" | custom-call | flops 67108864 | bytes 1573248 | tf_op jit(solution)/shard_map/pallas_call | solution.py:25
  23.8 3.2 %collective-permute-start.16 = (bf16[528,128]{1,0:T(8,128)(2,1)S(1)}, bf16[528,128]{1,0:T(8,128)(2,1)S(1)}, u32[]{:S(2)}, u32[]{:S(2)}) collective-permute-start(bf16[528,128]{1,0:T(8,128)(2,1)S(1)} %get-tuple-element.46), channel_id=1, source_target_pairs={{0,24},{8,16},{16,8},{24,0},{1,25},{9,17},{17,9},{25,1},{2,26},{10... | collective-permute-start | bytes 405512 | tf_op jit(solution)/shard_map/ppermute | solution.py:38
  27.1 1.6 %collective-permute-start.11 = (bf16[528,128]{1,0:T(8,128)(2,1)S(1)}, bf16[528,128]{1,0:T(8,128)(2,1)S(1)}, u32[]{:S(2)}, u32[]{:S(2)}) collective-permute-start(bf16[528,128]{1,0:T(8,128)(2,1)S(1)} %get-tuple-element.41), channel_id=1, source_target_pairs={{0,2},{1,3},{2,0},{3,1},{4,6},{5,7},{6,4},{7,5},{8,10},{9,11},{10,... | collective-permute-start | bytes 405512 | tf_op jit(solution)/shard_map/ppermute | solution.py:38
  28.7 0.8 collective-permute-start.12
  29.5 0.8 collective-permute-done.14.refs_7_
  30.3 1.9 %collective-permute-start.13 = (bf16[528,128]{1,0:T(8,128)(2,1)S(1)}, bf16[528,128]{1,0:T(8,128)(2,1)S(1)}, u32[]{:S(2)}, u32[]{:S(2)}) collective-permute-start(bf16[528,128]{1,0:T(8,128)(2,1)S(1)} %get-tuple-element.43), channel_id=1, source_target_pairs={{0,6},{1,7},{2,4},{3,5},{4,2},{5,3},{6,0},{7,1},{8,14},{9,15},{10,... | collective-permute-start | bytes 405512 | tf_op jit(solution)/shard_map/ppermute | solution.py:38
  32.3 3.9 %collective-permute-done.15.refs_8_ = bf16[528,128]{1,0:T(8,128)(2,1)S(1)} collective-permute-done((bf16[528,128]{1,0:T(8,128)(2,1)S(1)}, bf16[528,128]{1,0:T(8,128)(2,1)S(1)}, u32[]{:S(2)}, u32[]{:S(2)}) %collective-permute-start.15) | collective-permute-done | bytes 135200 | tf_op jit(solution)/shard_map/ppermute | solution.py:38
  36.8 2.7 %collective-permute-start.25 = (bf16[8,64,128]{2,1,0:T(8,128)(2,1)S(1)}, bf16[8,64,128]{2,1,0:T(8,128)(2,1)S(1)}, u32[]{:S(2)}, u32[]{:S(2)}) collective-permute-start(bf16[8,64,128]{2,1,0:T(8,128)(2,1)S(1)} %get-tuple-element.49.refs_2_.refs_3_), channel_id=1, source_target_pairs={{0,16},{8,24},{16,0},{24,8},{1,17},{9,25},{17,1},{25,9},{2,18},{10... | collective-permute-start | bytes 393224 | tf_op jit(solution)/shard_map/ppermute | solution.py:38
  39.5 2.5 %collective-permute-start.19 = (bf16[8,64,128]{2,1,0:T(8,128)(2,1)S(1)}, bf16[8,64,128]{2,1,0:T(8,128)(2,1)S(1)}, u32[]{:S(2)}, u32[]{:S(2)}) collective-permute-start(bf16[8,64,128]{2,1,0:T(8,128)(2,1)S(1)} %get-tuple-element.49.refs_2_.refs_3_), channel_id=1, source_target_pairs={{0,6},{1,7},{2,4},{3,5},{4,2},{5,3},{6,0},{7,1},{8,14},{9,15},{10,... | collective-permute-start | bytes 393224 | tf_op jit(solution)/shard_map/ppermute | solution.py:38
  43.1 1.9 %collective-permute-done.24.refs_5_ = bf16[7,64,128]{2,1,0:T(8,128)(2,1)S(1)} collective-permute-done((bf16[7,64,128]{2,1,0:T(8,128)(2,1)S(1)}, bf16[7,64,128]{2,1,0:T(8,128)(2,1)S(1)}, u32[]{:S(2)}, u32[]{:S(2)}) %collective-permute-start.24) | collective-permute-done | bytes 114720 | tf_op jit(solution)/shard_map/ppermute | solution.py:38
  45.2 1.3 %collective-permute-start.26 = (bf16[9,64,128]{2,1,0:T(8,128)(2,1)S(1)}, bf16[9,64,128]{2,1,0:T(8,128)(2,1)S(1)}, u32[]{:S(2)}, u32[]{:S(2)}) collective-permute-start(bf16[9,64,128]{2,1,0:T(8,128)(2,1)S(1)} %pad_maximum_fusion.1), channel_id=1, source_target_pairs={{0,8},{8,0},{16,24},{24,16},{1,9},{9,1},{17,25},{25,17},{2,10},{10... | collective-permute-start | bytes 442376 | tf_op jit(solution)/shard_map/ppermute | solution.py:38
  48.0 0.8 collective-permute-done.22.refs_8_
  49.0 1.1 %shard_map.65 = (f32[8,64,128]{2,1,0:T(8,128)S(1)}, bf16[512,128]{1,0:T(8,128)(2,1)S(1)}, bf16[512,128]{1,0:T(8,128)(2,1)S(1)}, bf16[512,128]{1,0:T(8,128)(2,1)S(1)}) custom-call(s32[3,32]{1,0:T(4,128)S(1)} %copy-done.4, bf16[32,128,128]{2,1,0:T(8,128)(2,1)S(1)} %bitcast.7, bf16[8,64,128]{2,1,0:T(8,128)(2,1)S(1)} %get-tuple-element.49.refs_2_.refs_3_, ...), custom_call_target="tpu_custom_call" | custom-call | flops 67108864 | bytes 2097536 | tf_op jit(solution)/shard_map/pallas_call | solution.py:25
  50.4 1.4 %shard_map.66 = (f32[64,64,128]{2,1,0:T(8,128)S(1)}, bf16[4,512,128]{2,1,0:T(8,128)(2,1)S(1)}) custom-call(f32[8,64,128]{2,1,0:T(8,128)S(1)} %get-tuple-element.50.refs_0_.refs_4_, s32[3,32]{1,0:T(4,128)S(1)} %copy-done.4, bf16[32,128,128]{2,1,0:T(8,128)(2,1)S(1)} %bitcast.8, bf16[8,64,128]{2,1,0:T(8,128)(2,1)S(1)} %get-tuple-element.49.refs_2_.refs_3_, ...), custom_call_target="tpu_custom_call" | custom-call | flops 67108864 | bytes 1573248 | tf_op jit(solution)/shard_map/pallas_call | solution.py:25
  52.0 2.0 %collective-permute-start.31 = (bf16[512,128]{1,0:T(8,128)(2,1)S(1)}, bf16[512,128]{1,0:T(8,128)(2,1)S(1)}, u32[]{:S(2)}, u32[]{:S(2)}) collective-permute-start(bf16[512,128]{1,0:T(8,128)(2,1)S(1)} %get-tuple-element.59), channel_id=1, source_target_pairs={{0,8},{8,0},{16,24},{24,16},{1,9},{9,1},{17,25},{25,17},{2,10},{10... | collective-permute-start | bytes 393224 | tf_op jit(solution)/shard_map/ppermute | solution.py:38
  54.5 1.9 %collective-permute-start.33 = (bf16[512,128]{1,0:T(8,128)(2,1)S(1)}, bf16[512,128]{1,0:T(8,128)(2,1)S(1)}, u32[]{:S(2)}, u32[]{:S(2)}) collective-permute-start(bf16[512,128]{1,0:T(8,128)(2,1)S(1)} %get-tuple-element.61), channel_id=1, source_target_pairs={{0,24},{8,16},{16,8},{24,0},{1,25},{9,17},{17,9},{25,1},{2,26},{10... | collective-permute-start | bytes 393224 | tf_op jit(solution)/shard_map/ppermute | solution.py:38
  56.6 1.5 %collective-permute-start.28 = (bf16[512,128]{1,0:T(8,128)(2,1)S(1)}, bf16[512,128]{1,0:T(8,128)(2,1)S(1)}, u32[]{:S(2)}, u32[]{:S(2)}) collective-permute-start(bf16[512,128]{1,0:T(8,128)(2,1)S(1)} %get-tuple-element.56), channel_id=1, source_target_pairs={{0,2},{1,3},{2,0},{3,1},{4,6},{5,7},{6,4},{7,5},{8,10},{9,11},{10,... | collective-permute-start | bytes 393224 | tf_op jit(solution)/shard_map/ppermute | solution.py:38
  58.1 1.4 %collective-permute-start.29 = (bf16[512,128]{1,0:T(8,128)(2,1)S(1)}, bf16[512,128]{1,0:T(8,128)(2,1)S(1)}, u32[]{:S(2)}, u32[]{:S(2)}) collective-permute-start(bf16[512,128]{1,0:T(8,128)(2,1)S(1)} %get-tuple-element.57), channel_id=1, source_target_pairs={{0,4},{1,5},{2,6},{3,7},{4,0},{5,1},{6,2},{7,3},{8,12},{9,13},{10,... | collective-permute-start | bytes 393224 | tf_op jit(solution)/shard_map/ppermute | solution.py:38
  59.5 2.5 %collective-permute-start.30 = (bf16[512,128]{1,0:T(8,128)(2,1)S(1)}, bf16[512,128]{1,0:T(8,128)(2,1)S(1)}, u32[]{:S(2)}, u32[]{:S(2)}) collective-permute-start(bf16[512,128]{1,0:T(8,128)(2,1)S(1)} %get-tuple-element.58), channel_id=1, source_target_pairs={{0,6},{1,7},{2,4},{3,5},{4,2},{5,3},{6,0},{7,1},{8,14},{9,15},{10,... | collective-permute-start | bytes 393224 | tf_op jit(solution)/shard_map/ppermute | solution.py:38
  61.9 5.0 %collective-permute-done.32.refs_9_ = bf16[512,128]{1,0:T(8,128)(2,1)S(1)} collective-permute-done((bf16[512,128]{1,0:T(8,128)(2,1)S(1)}, bf16[512,128]{1,0:T(8,128)(2,1)S(1)}, u32[]{:S(2)}, u32[]{:S(2)}) %collective-permute-start.32) | collective-permute-done | bytes 131104 | tf_op jit(solution)/shard_map/ppermute | solution.py:38
  67.2 2.6 %collective-permute-start.42 = (bf16[8,64,128]{2,1,0:T(8,128)(2,1)S(1)}, bf16[8,64,128]{2,1,0:T(8,128)(2,1)S(1)}, u32[]{:S(2)}, u32[]{:S(2)}) collective-permute-start(bf16[8,64,128]{2,1,0:T(8,128)(2,1)S(1)} %get-tuple-element.63.refs_2_.refs_3_), channel_id=1, source_target_pairs={{0,16},{8,24},{16,0},{24,8},{1,17},{9,25},{17,1},{25,9},{2,18},{10... | collective-permute-start | bytes 393224 | tf_op jit(solution)/shard_map/ppermute | solution.py:38
  69.8 1.8 %collective-permute-start.36 = (bf16[8,64,128]{2,1,0:T(8,128)(2,1)S(1)}, bf16[8,64,128]{2,1,0:T(8,128)(2,1)S(1)}, u32[]{:S(2)}, u32[]{:S(2)}) collective-permute-start(bf16[8,64,128]{2,1,0:T(8,128)(2,1)S(1)} %get-tuple-element.63.refs_2_.refs_3_), channel_id=1, source_target_pairs={{0,6},{1,7},{2,4},{3,5},{4,2},{5,3},{6,0},{7,1},{8,14},{9,15},{10,... | collective-permute-start | bytes 393224 | tf_op jit(solution)/shard_map/ppermute | solution.py:38
  71.6 1.1 %collective-permute-start.35 = (bf16[8,64,128]{2,1,0:T(8,128)(2,1)S(1)}, bf16[8,64,128]{2,1,0:T(8,128)(2,1)S(1)}, u32[]{:S(2)}, u32[]{:S(2)}) collective-permute-start(bf16[8,64,128]{2,1,0:T(8,128)(2,1)S(1)} %get-tuple-element.63.refs_2_.refs_3_), channel_id=1, source_target_pairs={{0,4},{1,5},{2,6},{3,7},{4,0},{5,1},{6,2},{7,3},{8,12},{9,13},{10,... | collective-permute-start | bytes 393224 | tf_op jit(solution)/shard_map/ppermute | solution.py:38
  74.1 1.4 %collective-permute-done.41.refs_5_ = bf16[7,64,128]{2,1,0:T(8,128)(2,1)S(1)} collective-permute-done((bf16[7,64,128]{2,1,0:T(8,128)(2,1)S(1)}, bf16[7,64,128]{2,1,0:T(8,128)(2,1)S(1)}, u32[]{:S(2)}, u32[]{:S(2)}) %collective-permute-start.41) | collective-permute-done | bytes 114720 | tf_op jit(solution)/shard_map/ppermute | solution.py:38
  75.9 1.0 collective-permute-start.43
  79.4 1.0 %shard_map.69.refs_1_ = bf16[64,4096]{1,0:T(8,128)(2,1)S(1)} custom-call(s32[3,32]{1,0:T(4,128)S(1)} %copy-done.4, bf16[32,128,128]{2,1,0:T(8,128)(2,1)S(1)} %bitcast.9, bf16[8,64,128]{2,1,0:T(8,128)(2,1)S(1)} %get-tuple-element.63.refs_2_.refs_3_, bf16[8,64,128]{2,1,0:T(8,128)(2,1)S(1)} %collective-permute-done.34.refs_3_, ...), custom_call_target="tpu_custom_call" | custom-call | flops 67108864 | bytes 2097536 | tf_op jit(solution)/shard_map/pallas_call | solution.py:25
  81.1 1.2 %shard_map.71 = f32[40,128]{1,0:T(8,128)S(1)} custom-call(s32[3,32]{1,0:T(4,128)S(1)} %copy-done.4, bf16[64,4096]{1,0:T(8,128)(2,1)S(1)} %shard_map.69.refs_1_, f32[64,128]{1,0:T(8,128)S(1)} %shard_map.70.refs_2_, bf16[8,64,128]{2,1,0:T(8,128)(2,1)S(1)} %get-tuple-element.63.refs_2_.refs_3_, bf16[8,64,128]{2,1,0:T(8,128)(2,1)S(1)} %collective-permute-done.42.refs_4_, ...), custom_call_target="tpu_custom_call" | custom-call | flops 33554432 | bytes 1081728 | tf_op jit(solution)/shard_map/pallas_call | solution.py:25
  82.3 1.2 %collective-permute-done.44 = f32[40,128]{1,0:T(8,128)S(1)} collective-permute-done((f32[40,128]{1,0:T(8,128)S(1)}, f32[40,128]{1,0:T(8,128)S(1)}, u32[]{:S(2)}, u32[]{:S(2)}) %collective-permute-start.44) | collective-permute-done | bytes 20512 | tf_op jit(solution)/shard_map/ppermute | solution.py:38
  83.5 1.4 %collective-permute-start.47 = (f32[40,128]{1,0:T(8,128)S(1)}, f32[40,128]{1,0:T(8,128)S(1)}, u32[]{:S(2)}, u32[]{:S(2)}) collective-permute-start(f32[40,128]{1,0:T(8,128)S(1)} %add.12), channel_id=1, source_target_pairs={{0,6},{1,7},{2,4},{3,5},{4,2},{5,3},{6,0},{7,1},{8,14},{9,15},{10,... | collective-permute-start | bytes 61448 | tf_op jit(solution)/shard_map/ppermute | solution.py:38
  84.9 1.1 %collective-permute-start.46 = (f32[40,128]{1,0:T(8,128)S(1)}, f32[40,128]{1,0:T(8,128)S(1)}, u32[]{:S(2)}, u32[]{:S(2)}) collective-permute-start(f32[40,128]{1,0:T(8,128)S(1)} %add.12), channel_id=1, source_target_pairs={{0,4},{1,5},{2,6},{3,7},{4,0},{5,1},{6,2},{7,3},{8,12},{9,13},{10,... | collective-permute-start | bytes 61448 | tf_op jit(solution)/shard_map/ppermute | solution.py:38
  86.0 1.0 collective-permute-start.45
  87.0 1.2 %collective-permute-done.47 = f32[40,128]{1,0:T(8,128)S(1)} collective-permute-done((f32[40,128]{1,0:T(8,128)S(1)}, f32[40,128]{1,0:T(8,128)S(1)}, u32[]{:S(2)}, u32[]{:S(2)}) %collective-permute-start.47) | collective-permute-done | bytes 20512 | tf_op jit(solution)/shard_map/ppermute | solution.py:38
  88.7 1.1 %collective-permute-done.45 = f32[40,128]{1,0:T(8,128)S(1)} collective-permute-done((f32[40,128]{1,0:T(8,128)S(1)}, f32[40,128]{1,0:T(8,128)S(1)}, u32[]{:S(2)}, u32[]{:S(2)}) %collective-permute-start.45) | collective-permute-done | bytes 20512 | tf_op jit(solution)/shard_map/ppermute | solution.py:38
  89.8 1.9 %collective-permute-start.50 = (f32[40,128]{1,0:T(8,128)S(1)}, f32[40,128]{1,0:T(8,128)S(1)}, u32[]{:S(2)}, u32[]{:S(2)}) collective-permute-start(f32[40,128]{1,0:T(8,128)S(1)} %add_add_fusion.refs_1_), channel_id=1, source_target_pairs={{0,24},{8,16},{16,8},{24,0},{1,25},{9,17},{17,9},{25,1},{2,26},{10... | collective-permute-start | bytes 61448 | tf_op jit(solution)/shard_map/ppermute | solution.py:38
  91.7 0.9 collective-permute-start.49
  92.6 1.6 %collective-permute-start.48 = (f32[40,128]{1,0:T(8,128)S(1)}, f32[40,128]{1,0:T(8,128)S(1)}, u32[]{:S(2)}, u32[]{:S(2)}) collective-permute-start(f32[40,128]{1,0:T(8,128)S(1)} %add_add_fusion.refs_1_), channel_id=1, source_target_pairs={{0,8},{8,0},{16,24},{24,16},{1,9},{9,1},{17,25},{25,17},{2,10},{10... | collective-permute-start | bytes 61448 | tf_op jit(solution)/shard_map/ppermute | solution.py:38
  94.3 1.2 %collective-permute-done.50.refs_4_ = f32[40,128]{1,0:T(8,128)S(1)} collective-permute-done((f32[40,128]{1,0:T(8,128)S(1)}, f32[40,128]{1,0:T(8,128)S(1)}, u32[]{:S(2)}, u32[]{:S(2)}) %collective-permute-start.50) | collective-permute-done | bytes 20512 | tf_op jit(solution)/shard_map/ppermute | solution.py:38
  95.5 1.2 %collective-permute-done.49.refs_3_ = f32[40,128]{1,0:T(8,128)S(1)} collective-permute-done((f32[40,128]{1,0:T(8,128)S(1)}, f32[40,128]{1,0:T(8,128)S(1)}, u32[]{:S(2)}, u32[]{:S(2)}) %collective-permute-start.49) | collective-permute-done | bytes 20512 | tf_op jit(solution)/shard_map/ppermute | solution.py:38
  96.6 3.8 %shard_map.72 = (f32[64,1024]{1,0:T(8,128)}, f32[64,64]{1,0:T(8,128)}) custom-call(f32[64,1024]{1,0:T(8,128)S(1)} %get-tuple-element.62.refs_0_, f32[40,128]{1,0:T(8,128)S(1)} %add_add_fusion.refs_1_, f32[40,128]{1,0:T(8,128)S(1)} %collective-permute-done.48.refs_2_, f32[40,128]{1,0:T(8,128)S(1)} %collective-permute-done.49.refs_3_, ...), custom_call_target="tpu_custom_call" | custom-call | bytes 344064 | tf_op jit(solution)/shard_map/pallas_call | solution.py:25
  (90 shorter events, 16.3 us)
Async XLA Ops:
  1.6 11.6 %collective-permute-start.8 = (bf16[8,64,128]{2,1,0:T(8,128)(2,1)S(1)}, bf16[8,64,128]{2,1,0:T(8,128)(2,1)S(1)}, u32[]{:S(2)}, u32[]{:S(2)}) collective-permute-start(bf16[8,64,128]{2,1,0:T(8,128)(2,1)S(1)} %shard_map.60.refs_2_.refs_3_), channel_id=1, source_target_pairs={{0,16},{8,24},{16,0},{24,8},{1,17},{9,25},{17,1},{25,9},{2,18},{10... | collective-permute-start | bytes 393224 | tf_op jit(solution)/shard_map/ppermute | solution.py:38
  5.7 7.4 %collective-permute-start.7 = (bf16[7,64,128]{2,1,0:T(8,128)(2,1)S(1)}, bf16[7,64,128]{2,1,0:T(8,128)(2,1)S(1)}, u32[]{:S(2)}, u32[]{:S(2)}) collective-permute-start(bf16[7,64,128]{2,1,0:T(8,128)(2,1)S(1)} %slice.24), channel_id=1, source_target_pairs={{0,8},{8,0},{16,24},{24,16},{1,9},{9,1},{17,25},{25,17},{2,10},{10... | collective-permute-start | bytes 344072 | tf_op jit(solution)/shard_map/ppermute | solution.py:38
  7.4 6.6 %collective-permute-start.2 = (bf16[8,64,128]{2,1,0:T(8,128)(2,1)S(1)}, bf16[8,64,128]{2,1,0:T(8,128)(2,1)S(1)}, u32[]{:S(2)}, u32[]{:S(2)}) collective-permute-start(bf16[8,64,128]{2,1,0:T(8,128)(2,1)S(1)} %shard_map.60.refs_2_.refs_3_), channel_id=1, source_target_pairs={{0,6},{1,7},{2,4},{3,5},{4,2},{5,3},{6,0},{7,1},{8,14},{9,15},{10,... | collective-permute-start | bytes 393224 | tf_op jit(solution)/shard_map/ppermute | solution.py:38
  9.8 5.9 %collective-permute-start.1 = (bf16[8,64,128]{2,1,0:T(8,128)(2,1)S(1)}, bf16[8,64,128]{2,1,0:T(8,128)(2,1)S(1)}, u32[]{:S(2)}, u32[]{:S(2)}) collective-permute-start(bf16[8,64,128]{2,1,0:T(8,128)(2,1)S(1)} %shard_map.60.refs_2_.refs_3_), channel_id=1, source_target_pairs={{0,4},{1,5},{2,6},{3,7},{4,0},{5,1},{6,2},{7,3},{8,12},{9,13},{10,... | collective-permute-start | bytes 393224 | tf_op jit(solution)/shard_map/ppermute | solution.py:38
  10.3 5.5 %collective-permute-start = (bf16[8,64,128]{2,1,0:T(8,128)(2,1)S(1)}, bf16[8,64,128]{2,1,0:T(8,128)(2,1)S(1)}, u32[]{:S(2)}, u32[]{:S(2)}) collective-permute-start(bf16[8,64,128]{2,1,0:T(8,128)(2,1)S(1)} %shard_map.60.refs_2_.refs_3_), channel_id=1, source_target_pairs={{0,2},{1,3},{2,0},{3,1},{4,6},{5,7},{6,4},{7,5},{8,10},{9,11},{10,... | collective-permute-start | bytes 393224 | tf_op jit(solution)/shard_map/ppermute | solution.py:38
  13.2 7.3 %collective-permute-start.9 = (bf16[9,64,128]{2,1,0:T(8,128)(2,1)S(1)}, bf16[9,64,128]{2,1,0:T(8,128)(2,1)S(1)}, u32[]{:S(2)}, u32[]{:S(2)}) collective-permute-start(bf16[9,64,128]{2,1,0:T(8,128)(2,1)S(1)} %pad_maximum_fusion), channel_id=1, source_target_pairs={{0,8},{8,0},{16,24},{24,16},{1,9},{9,1},{17,25},{25,17},{2,10},{10... | collective-permute-start | bytes 442376 | tf_op jit(solution)/shard_map/ppermute | solution.py:38
  13.7 2.6 %collective-permute-start.3 = (bf16[8,64,128]{2,1,0:T(8,128)(2,1)S(1)}, bf16[8,64,128]{2,1,0:T(8,128)(2,1)S(1)}, u32[]{:S(2)}, u32[]{:S(2)}) collective-permute-start(bf16[8,64,128]{2,1,0:T(8,128)(2,1)S(1)} %shard_map.60.refs_2_.refs_3_), channel_id=1, source_target_pairs={{0,1},{1,0},{2,3},{3,2},{4,5},{5,4},{6,7},{7,6},{8,9},{9,8},{10,11... | collective-permute-start | bytes 393224 | tf_op jit(solution)/shard_map/ppermute | solution.py:38
  13.9 2.3 %collective-permute-start.6 = (bf16[8,64,128]{2,1,0:T(8,128)(2,1)S(1)}, bf16[8,64,128]{2,1,0:T(8,128)(2,1)S(1)}, u32[]{:S(2)}, u32[]{:S(2)}) collective-permute-start(bf16[8,64,128]{2,1,0:T(8,128)(2,1)S(1)} %collective-permute-done.2.refs_5_), channel_id=1, source_target_pairs={{0,1},{1,0},{2,3},{3,2},{4,5},{5,4},{6,7},{7,6},{8,9},{9,8},{10,11... | collective-permute-start | bytes 393224 | tf_op jit(solution)/shard_map/ppermute | solution.py:38
  15.7 1.3 %collective-permute-start.5 = (bf16[8,64,128]{2,1,0:T(8,128)(2,1)S(1)}, bf16[8,64,128]{2,1,0:T(8,128)(2,1)S(1)}, u32[]{:S(2)}, u32[]{:S(2)}) collective-permute-start(bf16[8,64,128]{2,1,0:T(8,128)(2,1)S(1)} %collective-permute-done.1.refs_4_), channel_id=1, source_target_pairs={{0,1},{1,0},{2,3},{3,2},{4,5},{5,4},{6,7},{7,6},{8,9},{9,8},{10,11... | collective-permute-start | bytes 393224 | tf_op jit(solution)/shard_map/ppermute | solution.py:38
  15.8 1.4 %collective-permute-start.4 = (bf16[8,64,128]{2,1,0:T(8,128)(2,1)S(1)}, bf16[8,64,128]{2,1,0:T(8,128)(2,1)S(1)}, u32[]{:S(2)}, u32[]{:S(2)}) collective-permute-start(bf16[8,64,128]{2,1,0:T(8,128)(2,1)S(1)} %collective-permute-done.refs_3_), channel_id=1, source_target_pairs={{0,1},{1,0},{2,3},{3,2},{4,5},{5,4},{6,7},{7,6},{8,9},{9,8},{10,11... | collective-permute-start | bytes 393224 | tf_op jit(solution)/shard_map/ppermute | solution.py:38
  22.2 4.8 %collective-permute-start.10 = (bf16[4,528,128]{2,1,0:T(8,128)(2,1)S(1)}, bf16[4,528,128]{2,1,0:T(8,128)(2,1)S(1)}, u32[]{:S(2)}, u32[]{:S(2)}) collective-permute-start(bf16[4,528,128]{2,1,0:T(8,128)(2,1)S(1)} %get-tuple-element.38), channel_id=1, source_target_pairs={{0,1},{1,0},{2,3},{3,2},{4,5},{5,4},{6,7},{7,6},{8,9},{9,8},{10,11... | collective-permute-start | bytes 1622024 | tf_op jit(solution)/shard_map/ppermute | solution.py:38
  22.6 7.7 %collective-permute-start.14 = (bf16[528,128]{1,0:T(8,128)(2,1)S(1)}, bf16[528,128]{1,0:T(8,128)(2,1)S(1)}, u32[]{:S(2)}, u32[]{:S(2)}) collective-permute-start(bf16[528,128]{1,0:T(8,128)(2,1)S(1)} %get-tuple-element.44), channel_id=1, source_target_pairs={{0,8},{8,0},{16,24},{24,16},{1,9},{9,1},{17,25},{25,17},{2,10},{10... | collective-permute-start | bytes 405512 | tf_op jit(solution)/shard_map/ppermute | solution.py:38
  23.0 13.2 %collective-permute-start.15 = (bf16[528,128]{1,0:T(8,128)(2,1)S(1)}, bf16[528,128]{1,0:T(8,128)(2,1)S(1)}, u32[]{:S(2)}, u32[]{:S(2)}) collective-permute-start(bf16[528,128]{1,0:T(8,128)(2,1)S(1)} %get-tuple-element.45), channel_id=1, source_target_pairs={{0,16},{8,24},{16,0},{24,8},{1,17},{9,25},{17,1},{25,9},{2,18},{10... | collective-permute-start | bytes 405512 | tf_op jit(solution)/shard_map/ppermute | solution.py:38
  23.8 12.4 %collective-permute-start.16 = (bf16[528,128]{1,0:T(8,128)(2,1)S(1)}, bf16[528,128]{1,0:T(8,128)(2,1)S(1)}, u32[]{:S(2)}, u32[]{:S(2)}) collective-permute-start(bf16[528,128]{1,0:T(8,128)(2,1)S(1)} %get-tuple-element.46), channel_id=1, source_target_pairs={{0,24},{8,16},{16,8},{24,0},{1,25},{9,17},{17,9},{25,1},{2,26},{10... | collective-permute-start | bytes 405512 | tf_op jit(solution)/shard_map/ppermute | solution.py:38
  27.1 9.1 %collective-permute-start.11 = (bf16[528,128]{1,0:T(8,128)(2,1)S(1)}, bf16[528,128]{1,0:T(8,128)(2,1)S(1)}, u32[]{:S(2)}, u32[]{:S(2)}) collective-permute-start(bf16[528,128]{1,0:T(8,128)(2,1)S(1)} %get-tuple-element.41), channel_id=1, source_target_pairs={{0,2},{1,3},{2,0},{3,1},{4,6},{5,7},{6,4},{7,5},{8,10},{9,11},{10,... | collective-permute-start | bytes 405512 | tf_op jit(solution)/shard_map/ppermute | solution.py:38
  28.7 7.9 %collective-permute-start.12 = (bf16[528,128]{1,0:T(8,128)(2,1)S(1)}, bf16[528,128]{1,0:T(8,128)(2,1)S(1)}, u32[]{:S(2)}, u32[]{:S(2)}) collective-permute-start(bf16[528,128]{1,0:T(8,128)(2,1)S(1)} %get-tuple-element.42), channel_id=1, source_target_pairs={{0,4},{1,5},{2,6},{3,7},{4,0},{5,1},{6,2},{7,3},{8,12},{9,13},{10,... | collective-permute-start | bytes 405512 | tf_op jit(solution)/shard_map/ppermute | solution.py:38
  30.3 6.2 %collective-permute-start.13 = (bf16[528,128]{1,0:T(8,128)(2,1)S(1)}, bf16[528,128]{1,0:T(8,128)(2,1)S(1)}, u32[]{:S(2)}, u32[]{:S(2)}) collective-permute-start(bf16[528,128]{1,0:T(8,128)(2,1)S(1)} %get-tuple-element.43), channel_id=1, source_target_pairs={{0,6},{1,7},{2,4},{3,5},{4,2},{5,3},{6,0},{7,1},{8,14},{9,15},{10,... | collective-permute-start | bytes 405512 | tf_op jit(solution)/shard_map/ppermute | solution.py:38
  36.8 8.4 %collective-permute-start.25 = (bf16[8,64,128]{2,1,0:T(8,128)(2,1)S(1)}, bf16[8,64,128]{2,1,0:T(8,128)(2,1)S(1)}, u32[]{:S(2)}, u32[]{:S(2)}) collective-permute-start(bf16[8,64,128]{2,1,0:T(8,128)(2,1)S(1)} %get-tuple-element.49.refs_2_.refs_3_), channel_id=1, source_target_pairs={{0,16},{8,24},{16,0},{24,8},{1,17},{9,25},{17,1},{25,9},{2,18},{10... | collective-permute-start | bytes 393224 | tf_op jit(solution)/shard_map/ppermute | solution.py:38
  39.4 5.5 %collective-permute-start.24 = (bf16[7,64,128]{2,1,0:T(8,128)(2,1)S(1)}, bf16[7,64,128]{2,1,0:T(8,128)(2,1)S(1)}, u32[]{:S(2)}, u32[]{:S(2)}) collective-permute-start(bf16[7,64,128]{2,1,0:T(8,128)(2,1)S(1)} %slice.20), channel_id=1, source_target_pairs={{0,8},{8,0},{16,24},{24,16},{1,9},{9,1},{17,25},{25,17},{2,10},{10... | collective-permute-start | bytes 344072 | tf_op jit(solution)/shard_map/ppermute | solution.py:38
  39.5 7.1 %collective-permute-start.19 = (bf16[8,64,128]{2,1,0:T(8,128)(2,1)S(1)}, bf16[8,64,128]{2,1,0:T(8,128)(2,1)S(1)}, u32[]{:S(2)}, u32[]{:S(2)}) collective-permute-start(bf16[8,64,128]{2,1,0:T(8,128)(2,1)S(1)} %get-tuple-element.49.refs_2_.refs_3_), channel_id=1, source_target_pairs={{0,6},{1,7},{2,4},{3,5},{4,2},{5,3},{6,0},{7,1},{8,14},{9,15},{10,... | collective-permute-start | bytes 393224 | tf_op jit(solution)/shard_map/ppermute | solution.py:38
  42.0 5.5 %collective-permute-start.18 = (bf16[8,64,128]{2,1,0:T(8,128)(2,1)S(1)}, bf16[8,64,128]{2,1,0:T(8,128)(2,1)S(1)}, u32[]{:S(2)}, u32[]{:S(2)}) collective-permute-start(bf16[8,64,128]{2,1,0:T(8,128)(2,1)S(1)} %get-tuple-element.49.refs_2_.refs_3_), channel_id=1, source_target_pairs={{0,4},{1,5},{2,6},{3,7},{4,0},{5,1},{6,2},{7,3},{8,12},{9,13},{10,... | collective-permute-start | bytes 393224 | tf_op jit(solution)/shard_map/ppermute | solution.py:38
  42.5 5.0 %collective-permute-start.17 = (bf16[8,64,128]{2,1,0:T(8,128)(2,1)S(1)}, bf16[8,64,128]{2,1,0:T(8,128)(2,1)S(1)}, u32[]{:S(2)}, u32[]{:S(2)}) collective-permute-start(bf16[8,64,128]{2,1,0:T(8,128)(2,1)S(1)} %get-tuple-element.49.refs_2_.refs_3_), channel_id=1, source_target_pairs={{0,2},{1,3},{2,0},{3,1},{4,6},{5,7},{6,4},{7,5},{8,10},{9,11},{10,... | collective-permute-start | bytes 393224 | tf_op jit(solution)/shard_map/ppermute | solution.py:38
  45.2 5.2 %collective-permute-start.26 = (bf16[9,64,128]{2,1,0:T(8,128)(2,1)S(1)}, bf16[9,64,128]{2,1,0:T(8,128)(2,1)S(1)}, u32[]{:S(2)}, u32[]{:S(2)}) collective-permute-start(bf16[9,64,128]{2,1,0:T(8,128)(2,1)S(1)} %pad_maximum_fusion.1), channel_id=1, source_target_pairs={{0,8},{8,0},{16,24},{24,16},{1,9},{9,1},{17,25},{25,17},{2,10},{10... | collective-permute-start | bytes 442376 | tf_op jit(solution)/shard_map/ppermute | solution.py:38
  46.5 1.6 %collective-permute-start.20 = (bf16[8,64,128]{2,1,0:T(8,128)(2,1)S(1)}, bf16[8,64,128]{2,1,0:T(8,128)(2,1)S(1)}, u32[]{:S(2)}, u32[]{:S(2)}) collective-permute-start(bf16[8,64,128]{2,1,0:T(8,128)(2,1)S(1)} %get-tuple-element.49.refs_2_.refs_3_), channel_id=1, source_target_pairs={{0,1},{1,0},{2,3},{3,2},{4,5},{5,4},{6,7},{7,6},{8,9},{9,8},{10,11... | collective-permute-start | bytes 393224 | tf_op jit(solution)/shard_map/ppermute | solution.py:38
  46.6 1.4 %collective-permute-start.23 = (bf16[8,64,128]{2,1,0:T(8,128)(2,1)S(1)}, bf16[8,64,128]{2,1,0:T(8,128)(2,1)S(1)}, u32[]{:S(2)}, u32[]{:S(2)}) collective-permute-start(bf16[8,64,128]{2,1,0:T(8,128)(2,1)S(1)} %collective-permute-done.19.refs_5_), channel_id=1, source_target_pairs={{0,1},{1,0},{2,3},{3,2},{4,5},{5,4},{6,7},{7,6},{8,9},{9,8},{10,11... | collective-permute-start | bytes 393224 | tf_op jit(solution)/shard_map/ppermute | solution.py:38
  47.6 1.5 %collective-permute-start.21 = (bf16[8,64,128]{2,1,0:T(8,128)(2,1)S(1)}, bf16[8,64,128]{2,1,0:T(8,128)(2,1)S(1)}, u32[]{:S(2)}, u32[]{:S(2)}) collective-permute-start(bf16[8,64,128]{2,1,0:T(8,128)(2,1)S(1)} %collective-permute-done.17.refs_3_), channel_id=1, source_target_pairs={{0,1},{1,0},{2,3},{3,2},{4,5},{5,4},{6,7},{7,6},{8,9},{9,8},{10,11... | collective-permute-start | bytes 393224 | tf_op jit(solution)/shard_map/ppermute | solution.py:38
  51.8 4.6 %collective-permute-start.27 = (bf16[4,512,128]{2,1,0:T(8,128)(2,1)S(1)}, bf16[4,512,128]{2,1,0:T(8,128)(2,1)S(1)}, u32[]{:S(2)}, u32[]{:S(2)}) collective-permute-start(bf16[4,512,128]{2,1,0:T(8,128)(2,1)S(1)} %get-tuple-element.54), channel_id=1, source_target_pairs={{0,1},{1,0},{2,3},{3,2},{4,5},{5,4},{6,7},{7,6},{8,9},{9,8},{10,11... | collective-permute-start | bytes 1572872 | tf_op jit(solution)/shard_map/ppermute | solution.py:38
  52.0 7.4 %collective-permute-start.31 = (bf16[512,128]{1,0:T(8,128)(2,1)S(1)}, bf16[512,128]{1,0:T(8,128)(2,1)S(1)}, u32[]{:S(2)}, u32[]{:S(2)}) collective-permute-start(bf16[512,128]{1,0:T(8,128)(2,1)S(1)} %get-tuple-element.59), channel_id=1, source_target_pairs={{0,8},{8,0},{16,24},{24,16},{1,9},{9,1},{17,25},{25,17},{2,10},{10... | collective-permute-start | bytes 393224 | tf_op jit(solution)/shard_map/ppermute | solution.py:38
  54.1 12.9 %collective-permute-start.32 = (bf16[512,128]{1,0:T(8,128)(2,1)S(1)}, bf16[512,128]{1,0:T(8,128)(2,1)S(1)}, u32[]{:S(2)}, u32[]{:S(2)}) collective-permute-start(bf16[512,128]{1,0:T(8,128)(2,1)S(1)} %get-tuple-element.60), channel_id=1, source_target_pairs={{0,16},{8,24},{16,0},{24,8},{1,17},{9,25},{17,1},{25,9},{2,18},{10... | collective-permute-start | bytes 393224 | tf_op jit(solution)/shard_map/ppermute | solution.py:38
  54.5 12.4 %collective-permute-start.33 = (bf16[512,128]{1,0:T(8,128)(2,1)S(1)}, bf16[512,128]{1,0:T(8,128)(2,1)S(1)}, u32[]{:S(2)}, u32[]{:S(2)}) collective-permute-start(bf16[512,128]{1,0:T(8,128)(2,1)S(1)} %get-tuple-element.61), channel_id=1, source_target_pairs={{0,24},{8,16},{16,8},{24,0},{1,25},{9,17},{17,9},{25,1},{2,26},{10... | collective-permute-start | bytes 393224 | tf_op jit(solution)/shard_map/ppermute | solution.py:38
  56.6 10.4 %collective-permute-start.28 = (bf16[512,128]{1,0:T(8,128)(2,1)S(1)}, bf16[512,128]{1,0:T(8,128)(2,1)S(1)}, u32[]{:S(2)}, u32[]{:S(2)}) collective-permute-start(bf16[512,128]{1,0:T(8,128)(2,1)S(1)} %get-tuple-element.56), channel_id=1, source_target_pairs={{0,2},{1,3},{2,0},{3,1},{4,6},{5,7},{6,4},{7,5},{8,10},{9,11},{10,... | collective-permute-start | bytes 393224 | tf_op jit(solution)/shard_map/ppermute | solution.py:38
  58.1 8.9 %collective-permute-start.29 = (bf16[512,128]{1,0:T(8,128)(2,1)S(1)}, bf16[512,128]{1,0:T(8,128)(2,1)S(1)}, u32[]{:S(2)}, u32[]{:S(2)}) collective-permute-start(bf16[512,128]{1,0:T(8,128)(2,1)S(1)} %get-tuple-element.57), channel_id=1, source_target_pairs={{0,4},{1,5},{2,6},{3,7},{4,0},{5,1},{6,2},{7,3},{8,12},{9,13},{10,... | collective-permute-start | bytes 393224 | tf_op jit(solution)/shard_map/ppermute | solution.py:38
  59.5 7.5 %collective-permute-start.30 = (bf16[512,128]{1,0:T(8,128)(2,1)S(1)}, bf16[512,128]{1,0:T(8,128)(2,1)S(1)}, u32[]{:S(2)}, u32[]{:S(2)}) collective-permute-start(bf16[512,128]{1,0:T(8,128)(2,1)S(1)} %get-tuple-element.58), channel_id=1, source_target_pairs={{0,6},{1,7},{2,4},{3,5},{4,2},{5,3},{6,0},{7,1},{8,14},{9,15},{10,... | collective-permute-start | bytes 393224 | tf_op jit(solution)/shard_map/ppermute | solution.py:38
  67.2 8.7 %collective-permute-start.42 = (bf16[8,64,128]{2,1,0:T(8,128)(2,1)S(1)}, bf16[8,64,128]{2,1,0:T(8,128)(2,1)S(1)}, u32[]{:S(2)}, u32[]{:S(2)}) collective-permute-start(bf16[8,64,128]{2,1,0:T(8,128)(2,1)S(1)} %get-tuple-element.63.refs_2_.refs_3_), channel_id=1, source_target_pairs={{0,16},{8,24},{16,0},{24,8},{1,17},{9,25},{17,1},{25,9},{2,18},{10... | collective-permute-start | bytes 393224 | tf_op jit(solution)/shard_map/ppermute | solution.py:38
  69.8 5.7 %collective-permute-start.41 = (bf16[7,64,128]{2,1,0:T(8,128)(2,1)S(1)}, bf16[7,64,128]{2,1,0:T(8,128)(2,1)S(1)}, u32[]{:S(2)}, u32[]{:S(2)}) collective-permute-start(bf16[7,64,128]{2,1,0:T(8,128)(2,1)S(1)} %slice.22), channel_id=1, source_target_pairs={{0,8},{8,0},{16,24},{24,16},{1,9},{9,1},{17,25},{25,17},{2,10},{10... | collective-permute-start | bytes 344072 | tf_op jit(solution)/shard_map/ppermute | solution.py:38
  69.8 7.1 %collective-permute-start.36 = (bf16[8,64,128]{2,1,0:T(8,128)(2,1)S(1)}, bf16[8,64,128]{2,1,0:T(8,128)(2,1)S(1)}, u32[]{:S(2)}, u32[]{:S(2)}) collective-permute-start(bf16[8,64,128]{2,1,0:T(8,128)(2,1)S(1)} %get-tuple-element.63.refs_2_.refs_3_), channel_id=1, source_target_pairs={{0,6},{1,7},{2,4},{3,5},{4,2},{5,3},{6,0},{7,1},{8,14},{9,15},{10,... | collective-permute-start | bytes 393224 | tf_op jit(solution)/shard_map/ppermute | solution.py:38
  71.6 6.2 %collective-permute-start.35 = (bf16[8,64,128]{2,1,0:T(8,128)(2,1)S(1)}, bf16[8,64,128]{2,1,0:T(8,128)(2,1)S(1)}, u32[]{:S(2)}, u32[]{:S(2)}) collective-permute-start(bf16[8,64,128]{2,1,0:T(8,128)(2,1)S(1)} %get-tuple-element.63.refs_2_.refs_3_), channel_id=1, source_target_pairs={{0,4},{1,5},{2,6},{3,7},{4,0},{5,1},{6,2},{7,3},{8,12},{9,13},{10,... | collective-permute-start | bytes 393224 | tf_op jit(solution)/shard_map/ppermute | solution.py:38
  72.7 5.1 %collective-permute-start.34 = (bf16[8,64,128]{2,1,0:T(8,128)(2,1)S(1)}, bf16[8,64,128]{2,1,0:T(8,128)(2,1)S(1)}, u32[]{:S(2)}, u32[]{:S(2)}) collective-permute-start(bf16[8,64,128]{2,1,0:T(8,128)(2,1)S(1)} %get-tuple-element.63.refs_2_.refs_3_), channel_id=1, source_target_pairs={{0,2},{1,3},{2,0},{3,1},{4,6},{5,7},{6,4},{7,5},{8,10},{9,11},{10,... | collective-permute-start | bytes 393224 | tf_op jit(solution)/shard_map/ppermute | solution.py:38
  75.9 5.2 %collective-permute-start.43 = (bf16[9,64,128]{2,1,0:T(8,128)(2,1)S(1)}, bf16[9,64,128]{2,1,0:T(8,128)(2,1)S(1)}, u32[]{:S(2)}, u32[]{:S(2)}) collective-permute-start(bf16[9,64,128]{2,1,0:T(8,128)(2,1)S(1)} %pad_maximum_fusion.2), channel_id=1, source_target_pairs={{0,8},{8,0},{16,24},{24,16},{1,9},{9,1},{17,25},{25,17},{2,10},{10... | collective-permute-start | bytes 442376 | tf_op jit(solution)/shard_map/ppermute | solution.py:38
  76.8 1.5 %collective-permute-start.37 = (bf16[8,64,128]{2,1,0:T(8,128)(2,1)S(1)}, bf16[8,64,128]{2,1,0:T(8,128)(2,1)S(1)}, u32[]{:S(2)}, u32[]{:S(2)}) collective-permute-start(bf16[8,64,128]{2,1,0:T(8,128)(2,1)S(1)} %get-tuple-element.63.refs_2_.refs_3_), channel_id=1, source_target_pairs={{0,1},{1,0},{2,3},{3,2},{4,5},{5,4},{6,7},{7,6},{8,9},{9,8},{10,11... | collective-permute-start | bytes 393224 | tf_op jit(solution)/shard_map/ppermute | solution.py:38
  77.0 1.4 %collective-permute-start.40 = (bf16[8,64,128]{2,1,0:T(8,128)(2,1)S(1)}, bf16[8,64,128]{2,1,0:T(8,128)(2,1)S(1)}, u32[]{:S(2)}, u32[]{:S(2)}) collective-permute-start(bf16[8,64,128]{2,1,0:T(8,128)(2,1)S(1)} %collective-permute-done.36.refs_5_), channel_id=1, source_target_pairs={{0,1},{1,0},{2,3},{3,2},{4,5},{5,4},{6,7},{7,6},{8,9},{9,8},{10,11... | collective-permute-start | bytes 393224 | tf_op jit(solution)/shard_map/ppermute | solution.py:38
  77.8 1.5 %collective-permute-start.38 = (bf16[8,64,128]{2,1,0:T(8,128)(2,1)S(1)}, bf16[8,64,128]{2,1,0:T(8,128)(2,1)S(1)}, u32[]{:S(2)}, u32[]{:S(2)}) collective-permute-start(bf16[8,64,128]{2,1,0:T(8,128)(2,1)S(1)} %collective-permute-done.34.refs_3_), channel_id=1, source_target_pairs={{0,1},{1,0},{2,3},{3,2},{4,5},{5,4},{6,7},{7,6},{8,9},{9,8},{10,11... | collective-permute-start | bytes 393224 | tf_op jit(solution)/shard_map/ppermute | solution.py:38
  83.5 4.7 %collective-permute-start.47 = (f32[40,128]{1,0:T(8,128)S(1)}, f32[40,128]{1,0:T(8,128)S(1)}, u32[]{:S(2)}, u32[]{:S(2)}) collective-permute-start(f32[40,128]{1,0:T(8,128)S(1)} %add.12), channel_id=1, source_target_pairs={{0,6},{1,7},{2,4},{3,5},{4,2},{5,3},{6,0},{7,1},{8,14},{9,15},{10,... | collective-permute-start | bytes 61448 | tf_op jit(solution)/shard_map/ppermute | solution.py:38
  84.9 3.8 %collective-permute-start.46 = (f32[40,128]{1,0:T(8,128)S(1)}, f32[40,128]{1,0:T(8,128)S(1)}, u32[]{:S(2)}, u32[]{:S(2)}) collective-permute-start(f32[40,128]{1,0:T(8,128)S(1)} %add.12), channel_id=1, source_target_pairs={{0,4},{1,5},{2,6},{3,7},{4,0},{5,1},{6,2},{7,3},{8,12},{9,13},{10,... | collective-permute-start | bytes 61448 | tf_op jit(solution)/shard_map/ppermute | solution.py:38
  86.0 3.8 %collective-permute-start.45 = (f32[40,128]{1,0:T(8,128)S(1)}, f32[40,128]{1,0:T(8,128)S(1)}, u32[]{:S(2)}, u32[]{:S(2)}) collective-permute-start(f32[40,128]{1,0:T(8,128)S(1)} %add.12), channel_id=1, source_target_pairs={{0,2},{1,3},{2,0},{3,1},{4,6},{5,7},{6,4},{7,5},{8,10},{9,11},{10,... | collective-permute-start | bytes 61448 | tf_op jit(solution)/shard_map/ppermute | solution.py:38
  89.8 5.6 %collective-permute-start.50 = (f32[40,128]{1,0:T(8,128)S(1)}, f32[40,128]{1,0:T(8,128)S(1)}, u32[]{:S(2)}, u32[]{:S(2)}) collective-permute-start(f32[40,128]{1,0:T(8,128)S(1)} %add_add_fusion.refs_1_), channel_id=1, source_target_pairs={{0,24},{8,16},{16,8},{24,0},{1,25},{9,17},{17,9},{25,1},{2,26},{10... | collective-permute-start | bytes 61448 | tf_op jit(solution)/shard_map/ppermute | solution.py:38
  91.7 4.9 %collective-permute-start.49 = (f32[40,128]{1,0:T(8,128)S(1)}, f32[40,128]{1,0:T(8,128)S(1)}, u32[]{:S(2)}, u32[]{:S(2)}) collective-permute-start(f32[40,128]{1,0:T(8,128)S(1)} %add_add_fusion.refs_1_), channel_id=1, source_target_pairs={{0,16},{8,24},{16,0},{24,8},{1,17},{9,25},{17,1},{25,9},{2,18},{10... | collective-permute-start | bytes 61448 | tf_op jit(solution)/shard_map/ppermute | solution.py:38
  92.6 4.0 %collective-permute-start.48 = (f32[40,128]{1,0:T(8,128)S(1)}, f32[40,128]{1,0:T(8,128)S(1)}, u32[]{:S(2)}, u32[]{:S(2)}) collective-permute-start(f32[40,128]{1,0:T(8,128)S(1)} %add_add_fusion.refs_1_), channel_id=1, source_target_pairs={{0,8},{8,0},{16,24},{24,16},{1,9},{9,1},{17,25},{25,17},{2,10},{10... | collective-permute-start | bytes 61448 | tf_op jit(solution)/shard_map/ppermute | solution.py:38
  (8 other events, 44.9 us)

commit v16 on v15

--- a/solution.py
+++ b/solution.py
@@ -20,14 +20,15 @@
 DEGREE_ROWS = 16
 
 
-def call(kernel, out_shape, scratch, limit, args, flops=0, smem=0, after=()):
+def call(kernel, out_shape, scratch, limit, args, flops=0, smem=0, after=(), aliases={}):
     moved = sum(x.size * x.dtype.itemsize for x in args)
     return pl.pallas_call(
         lambda *refs: kernel(*refs[len(after) :]),
-        out_shape=out_shape,
+        out_shape=jax.tree.map(lambda x: jax.ShapeDtypeStruct(x.shape, x.dtype), out_shape),
         in_specs=[ANY] * len(after) + [SMEM] * smem + [VMEM] * (len(args) - smem),
         out_specs=jax.tree.map(lambda _: VMEM, out_shape),
         scratch_shapes=scratch,
+        input_output_aliases=aliases,
         compiler_params=pltpu.CompilerParams(vmem_limit_bytes=limit * 2**20),
         cost_estimate=pl.CostEstimate(flops=flops, bytes_accessed=moved, transcendentals=0),
     )(*after, *args)
@@ -70,15 +71,14 @@
             at += count
 
 
-def table_kernel(group, meta, tile_rows, tile_cols, table):
-    for t in range(table.shape[1]):
-        row, col = tile_rows[t], tile_cols[t]
-        apart = lax.div(row, group) ^ meta[1]
-        halves = lax.rem(apart, 2) * meta[2] + lax.div(apart, 2)
-        inside = lax.rem(row, group)
-        table[0, t] = (lax.div(col, group) ^ meta[0]) * group + lax.rem(col, group)
-        table[1, t] = apart * group + inside
-        table[2, t] = halves * group + inside
+def table_kernel(group, meta, rows_ref, cols_ref, table):
+    rows, cols = rows_ref[...], cols_ref[...]
+    apart = lax.div(rows, group) ^ meta[1]
+    halves = lax.rem(apart, 2) * meta[2] + lax.div(apart, 2)
+    inside = lax.rem(rows, group)
+    table[0:1, :] = (lax.div(cols, group) ^ meta[0]) * group + lax.rem(cols, group)
+    table[1:2, :] = apart * group + inside
+    table[2:3, :] = halves * group + inside
 
 
 def fill_ones(panel, vectors_n):
@@ -93,12 +93,16 @@
     )
 
 
+def zero_kernel(*refs):
+    for ref in refs:
+        ref[...] = jnp.zeros_like(ref)
+
+
 def column_kernel(runs, table, tiles_ref, *refs):
-    parts, (own_ref, *send_refs, panel, total) = refs[: len(runs)], refs[len(runs) :]
+    parts, (_, own_ref, total, *send_refs, panel) = refs[: len(runs)], refs[len(runs) :]
     group, vectors_n, _ = parts[0].shape
     fill(panel, parts, runs)
     fill_ones(panel, vectors_n)
-    total[...] = jnp.zeros_like(total)
     for t in range(tiles_ref.shape[0]):
         total[table[0, t]] += lax.dot_general(
             panel[table[1, t]], tiles_ref[t], NN, preferred_element_type=F32
@@ -109,12 +113,11 @@
 
 
 def row_kernel(runs, table, tiles_ref, *refs):
-    parts, (total, swap_ref, panel) = refs[: len(runs)], refs[len(runs) :]
+    parts, (_, total, swap_ref, panel) = refs[: len(runs)], refs[len(runs) :]
     group, vectors_n, _ = parts[0].shape
     half = swap_ref.shape[0]
     fill(panel, parts, runs)
     fill_ones(panel, vectors_n)
-    total[...] = jnp.zeros_like(total)
     for t in range(tiles_ref.shape[0]):
         total[table[2, t]] += lax.dot_general(
             panel[table[0, t]], tiles_ref[t], NT, preferred_element_type=F32
@@ -130,7 +133,7 @@
         send[group * vectors_n :, :] = split_degree(degree_of(total, start, group, vectors_n))
 
 
-def products(tiles, table, col_parts, row_parts, runs, degree):
+def products(tiles, table, col_parts, row_parts, zeros, runs, degree):
     group, vectors_n, width = col_parts[0].shape
     half = len(row_parts) // 2
     rows_n = max(place + count for run in runs[0] for place, count in run) // group
@@ -142,27 +145,27 @@
     def panel(count):
         return pltpu.VMEM((count * group, height, width), BF16)
 
-    col_own, *col_send = call(
+    col_own, _, *col_send = call(
         functools.partial(column_kernel, runs[1]),
-        [jax.ShapeDtypeStruct((group, height, width), F32)] + [send_shape] * (rows_n - 1),
-        [panel(2 * half), pltpu.VMEM((rows_n * group, height, width), F32)],
-        24,
-        [table, tiles, *row_parts],
+        [jax.ShapeDtypeStruct((group, height, width), F32), zeros[1]] + [send_shape] * (rows_n - 1),
+        [panel(2 * half)],
+        24,
+        [table, tiles, *row_parts, zeros[1]],
         flops,
         1,
+        (),
+        {2 + len(row_parts): 1},
     )
     kept, swap = call(
         functools.partial(row_kernel, runs[0]),
-        [
-            jax.ShapeDtypeStruct((2 * half * group, height, width), F32),
-            jax.ShapeDtypeStruct((half, rows, width), BF16),
-        ],
+        [zeros[0], jax.ShapeDtypeStruct((half, rows, width), BF16)],
         [panel(rows_n)],
         24,
-        [table, tiles, *col_parts],
+        [table, tiles, *col_parts, zeros[0]],
         flops,
         1,
         [col_own],
+        {3 + len(col_parts): 0},
     )
     return kept, swap, col_own, col_send
 
@@ -341,13 +344,14 @@
     projected = lower + lower.T + jnp.where(row == col, diagonal, 0.0)
     inverse = inverse_factor(gram)
 
-    def dot(a, b, dims):
-        return lax.dot_general(a, b, dims, precision=HIGHEST, preferred_element_type=F32)
+    def dot(a, b, dims, precision=HIGHEST):
+        return lax.dot_general(a, b, dims, precision=precision, preferred_element_type=F32)
 
     half_way = dot(inverse, projected, NN)
     rayleigh_ref[...] = dot(half_way, inverse, NT)
     turned = dot(inverse, half_way, NT)
-    ritz_ref[...] = dot(turned, dot(inverse, filtered_ref[...], NN), NN)
+    block = dot(inverse, filtered_ref[...], NN, lax.Precision.HIGH)
+    ritz_ref[...] = dot(turned, block, NN, lax.Precision.HIGH)
 
 
 def tree_sum(parts):
@@ -380,7 +384,8 @@
         cut = group - late
         passed = [((p // group ^ d) * group + p % group, n) for run in col_runs[1:] for p, n in run]
         col_runs += [[(d * group, cut)], [(d * group + cut, late), *passed]]
-    row_runs = [[((2 * d + core) * group, group)] for core in range(2) for d in range(chips_n)]
+    chip_order = [0, *range(chips_n - 1, 0, -1)]
+    row_runs = [[((2 * d + core) * group, group)] for core in range(2) for d in chip_order]
     runs = (col_runs, row_runs)
     def gather(rounded, first=()):
         held = [rounded]
@@ -392,27 +397,37 @@
             near, *passed = lax.optimization_barrier((near, *held[1:], *first))
             held[1:] = passed[: len(held) - 1]
             held += [near, trade(jnp.concatenate([rounded[group - late :], *held[1:]]), "row", d)]
-        chips = [rounded, *exchange([rounded] * (chips_n - 1), "col", 2)]
+        chips = [rounded, *exchange([rounded] * (chips_n - 1), "col", 2)[::-1]]
         return held, chips + [trade(chip, "col", 1) for chip in chips]
 
     def apply(rounded, table, degree, first=()):
-        kept, swap, col_own, col_send = products(
-            tiles, table, *gather(rounded, first), runs, degree
+        height = vectors_n + (DEGREE_ROWS if degree else 0)
+        zeros = call(
+            zero_kernel,
+            [jax.ShapeDtypeStruct((n * group, height, width), F32) for n in (cols_n, rows_n)],
+            [],
+            16,
+            [],
+            4 * total_nodes * vectors_n,
         )
+        parts = gather(rounded, (*first, *zeros))
+        kept, swap, col_own, col_send = products(tiles, table, *parts, zeros, runs, degree)
         col_got = exchange(col_send, "row")
         row_own, *row_send = merge(kept, trade(swap, "col", 1), vectors_n, degree)
         row_degree = row_send[:1] if degree else []
-        row_got = exchange(row_send[len(row_degree) :], "col", 2)
+        row_got = exchange(row_send[len(row_degree) :], "col", 2)[::-1]
         return [*row_degree, row_own, col_own, *row_got, *col_got]
 
     rounded = call(round_kernel, rounded_shape, [], 16, [start])
     meta = jnp.stack([lax.axis_index("row"), lax.axis_index("col"), chips_n]).astype(jnp.int32)
-    table = pl.pallas_call(
+    table = call(
         functools.partial(table_kernel, group),
-        out_shape=jax.ShapeDtypeStruct((3, tiles.shape[0]), jnp.int32),
-        in_specs=[SMEM] * 3,
-        out_specs=SMEM,
-    )(meta, tile_rows, tile_cols)
+        jax.ShapeDtypeStruct((3, tiles.shape[0]), jnp.int32),
+        [],
+        16,
+        [meta, tile_rows[None], tile_cols[None]],
+        smem=1,
+    )
     first, rounded, degree = call(
         functools.partial(first_kernel, chips_n),
         [vector_shape, rounded_shape, degree_shape],

time: 101 us -> 102 us (level)
  waiting for transfers between devices: 27.4 us -> 30.2 us
    ppermute x51, waiting for transfers between devices: 27.4 us -> 30.2 us  [trade(): return lax.ppermute(part, axis, [(i, i ^ d) for i in range(n)])]
    pallas_call x14 -> x16, Pallas kernels: 14.4 us -> 13.5 us  [call(): pl.pallas_call(lambda *refs: kernel(*refs[len(after):]), out_shape=jax.tr...]
    unnamed x10 -> x12, local copies, waits for them, and re-layouts: 2.86 us -> 3.49 us
  transfers between devices with their start and end apart: 51 -> 51, of which waited for: 30 -> 30; matrix products, arithmetic and copies ran while one was open for 1% -> 0% of each run, Pallas kernels for 6% -> 5%
where the time goes in v16:
time: 102 us
  starting transfers between devices  53.5 us (52%)
  waiting for transfers between devices  30.2 us (30%)
  Pallas kernels  13.5 us (13%)
  local copies, waits for them, and re-layouts  3.52 us (3%)
    ppermute x51, starting transfers between devices, trade(): return lax.ppermute(part, axis, [(i, i ^ d) for i in range(n)])  53.5 us
    ppermute x51, waiting for transfers between devices, trade(): return lax.ppermute(part, axis, [(i, i ^ d) for i in range(n)])  30.2 us
    pallas_call x16, Pallas kernels, call(): pl.pallas_call(lambda *refs: kernel(*refs[len(after):]), out_shape=jax.tr...  13.5 us
    unnamed x12, local copies, waits for them, and re-layouts  3.49 us
  transfers between devices with their start and end apart: 51, of which 30 were waited for; matrix products, arithmetic and copies ran while one was open for 0% of the time, Pallas kernels for 5%

profile of v16, /device:TPU:0, one launch (start us, length us, event | category | flops | bytes accessed | tf_op | source)
XLA Modules:
  0.0 101.7 jit_solution(4394289288189967005)
XLA Ops:
  0.6 0.9 copy-done.2
  1.6 4.1 %collective-permute-start.8 = (bf16[8,64,128]{2,1,0:T(8,128)(2,1)S(1)}, bf16[8,64,128]{2,1,0:T(8,128)(2,1)S(1)}, u32[]{:S(2)}, u32[]{:S(2)}) collective-permute-start(bf16[8,64,128]{2,1,0:T(8,128)(2,1)S(1)} %shard_map.60.refs_2_.refs_3_), channel_id=1, source_target_pairs={{0,16},{8,24},{16,0},{24,8},{1,17},{9,25},{17,1},{25,9},{2,18},{10... | collective-permute-start | bytes 393224 | tf_op jit(solution)/shard_map/ppermute | solution.py:39
  5.7 1.6 %collective-permute-start.7 = (bf16[7,64,128]{2,1,0:T(8,128)(2,1)S(1)}, bf16[7,64,128]{2,1,0:T(8,128)(2,1)S(1)}, u32[]{:S(2)}, u32[]{:S(2)}) collective-permute-start(bf16[7,64,128]{2,1,0:T(8,128)(2,1)S(1)} %slice.24), channel_id=1, source_target_pairs={{0,8},{8,0},{16,24},{24,16},{1,9},{9,1},{17,25},{25,17},{2,10},{10... | collective-permute-start | bytes 344072 | tf_op jit(solution)/shard_map/ppermute | solution.py:39
  7.4 2.4 %collective-permute-start = (bf16[8,64,128]{2,1,0:T(8,128)(2,1)S(1)}, bf16[8,64,128]{2,1,0:T(8,128)(2,1)S(1)}, u32[]{:S(2)}, u32[]{:S(2)}) collective-permute-start(bf16[8,64,128]{2,1,0:T(8,128)(2,1)S(1)} %shard_map.60.refs_2_.refs_3_), channel_id=1, source_target_pairs={{0,6},{1,7},{2,4},{3,5},{4,2},{5,3},{6,0},{7,1},{8,14},{9,15},{10,... | collective-permute-start | bytes 393224 | tf_op jit(solution)/shard_map/ppermute | solution.py:39
  14.1 1.6 %collective-permute-done.1.refs_4_ = bf16[8,64,128]{2,1,0:T(8,128)(2,1)S(1)} collective-permute-done((bf16[8,64,128]{2,1,0:T(8,128)(2,1)S(1)}, bf16[8,64,128]{2,1,0:T(8,128)(2,1)S(1)}, u32[]{:S(2)}, u32[]{:S(2)}) %collective-permute-start.1) | collective-permute-done | bytes 131104 | tf_op jit(solution)/shard_map/ppermute | solution.py:39
  16.3 0.8 collective-permute-done.5.refs_8_
  17.3 1.2 %copy-done = bf16[1,1,32,128,128]{4,3,2,1,0:T(8,128)(2,1)S(1)} copy-done((bf16[1,1,32,128,128]{4,3,2,1,0:T(8,128)(2,1)S(1)}, bf16[1,1,32,128,128]{4,3,2,1,0:T(8,128)(2,1)}, u32[]{:S(2)}) %copy-start) | copy-done | bytes 1048600
  18.5 1.2 %shard_map.62 = (f32[8,80,128]{2,1,0:T(8,128)S(1)}, f32[32,80,128]{2,1,0:T(8,128)S(1)}, bf16[528,128]{1,0:T(8,128)(2,1)S(1)}, bf16[528,128]{1,0:T(8,128)(2,1)S(1)}, bf16[528,128]{1,0:T(8,128)(2,1)S(1)}) custom-call(s32[3,32]{1,0:T(4,128)S(1)} %shard_map.59.refs_0_.refs_1_, bf16[32,128,128]{2,1,0:T(8,128)(2,1)S(1)} %bitcast.5, ...), custom_call_target="tpu_custom_call", output_to_operand_aliasing={{1}: (10, {})} | custom-call | flops 67108864 | bytes 3408256 | tf_op jit(solution)/shard_map/pallas_call | solution.py:25
  19.8 1.5 %shard_map.63 = (f32[64,80,128]{2,1,0:T(8,128)S(1)}, bf16[4,528,128]{2,1,0:T(8,128)(2,1)S(1)}) custom-call(f32[8,80,128]{2,1,0:T(8,128)S(1)} %get-tuple-element.39.refs_0_.refs_3_, s32[3,32]{1,0:T(4,128)S(1)} %shard_map.59.refs_0_.refs_1_, bf16[32,128,128]{2,1,0:T(8,128)(2,1)S(1)} %bitcast.6, ...), custom_call_target="tpu_custom_call", output_to_operand_aliasing={{0}: (7, {})} | custom-call | flops 67108864 | bytes 4194688 | tf_op jit(solution)/shard_map/pallas_call | solution.py:25
  22.1 1.5 %collective-permute-start.15 = (bf16[528,128]{1,0:T(8,128)(2,1)S(1)}, bf16[528,128]{1,0:T(8,128)(2,1)S(1)}, u32[]{:S(2)}, u32[]{:S(2)}) collective-permute-start(bf16[528,128]{1,0:T(8,128)(2,1)S(1)} %get-tuple-element.51), channel_id=1, source_target_pairs={{0,16},{8,24},{16,0},{24,8},{1,17},{9,25},{17,1},{25,9},{2,18},{10... | collective-permute-start | bytes 405512 | tf_op jit(solution)/shard_map/ppermute | solution.py:39
  23.6 2.4 %collective-permute-start.16 = (bf16[528,128]{1,0:T(8,128)(2,1)S(1)}, bf16[528,128]{1,0:T(8,128)(2,1)S(1)}, u32[]{:S(2)}, u32[]{:S(2)}) collective-permute-start(bf16[528,128]{1,0:T(8,128)(2,1)S(1)} %get-tuple-element.52), channel_id=1, source_target_pairs={{0,24},{8,16},{16,8},{24,0},{1,25},{9,17},{17,9},{25,1},{2,26},{10... | collective-permute-start | bytes 405512 | tf_op jit(solution)/shard_map/ppermute | solution.py:39
  26.2 1.8 %collective-permute-start.11 = (bf16[528,128]{1,0:T(8,128)(2,1)S(1)}, bf16[528,128]{1,0:T(8,128)(2,1)S(1)}, u32[]{:S(2)}, u32[]{:S(2)}) collective-permute-start(bf16[528,128]{1,0:T(8,128)(2,1)S(1)} %get-tuple-element.47), channel_id=1, source_target_pairs={{0,6},{1,7},{2,4},{3,5},{4,2},{5,3},{6,0},{7,1},{8,14},{9,15},{10,... | collective-permute-start | bytes 405512 | tf_op jit(solution)/shard_map/ppermute | solution.py:39
  28.0 1.2 %collective-permute-start.12 = (bf16[528,128]{1,0:T(8,128)(2,1)S(1)}, bf16[528,128]{1,0:T(8,128)(2,1)S(1)}, u32[]{:S(2)}, u32[]{:S(2)}) collective-permute-start(bf16[528,128]{1,0:T(8,128)(2,1)S(1)} %get-tuple-element.48), channel_id=1, source_target_pairs={{0,4},{1,5},{2,6},{3,7},{4,0},{5,1},{6,2},{7,3},{8,12},{9,13},{10,... | collective-permute-start | bytes 405512 | tf_op jit(solution)/shard_map/ppermute | solution.py:39
  29.4 1.5 %collective-permute-start.13 = (bf16[528,128]{1,0:T(8,128)(2,1)S(1)}, bf16[528,128]{1,0:T(8,128)(2,1)S(1)}, u32[]{:S(2)}, u32[]{:S(2)}) collective-permute-start(bf16[528,128]{1,0:T(8,128)(2,1)S(1)} %get-tuple-element.49), channel_id=1, source_target_pairs={{0,2},{1,3},{2,0},{3,1},{4,6},{5,7},{6,4},{7,5},{8,10},{9,11},{10,... | collective-permute-start | bytes 405512 | tf_op jit(solution)/shard_map/ppermute | solution.py:39
  30.9 4.4 %collective-permute-done.15.refs_8_ = bf16[528,128]{1,0:T(8,128)(2,1)S(1)} collective-permute-done((bf16[528,128]{1,0:T(8,128)(2,1)S(1)}, bf16[528,128]{1,0:T(8,128)(2,1)S(1)}, u32[]{:S(2)}, u32[]{:S(2)}) %collective-permute-start.15) | collective-permute-done | bytes 135200 | tf_op jit(solution)/shard_map/ppermute | solution.py:39
  35.5 3.0 %collective-permute-start.25 = (bf16[8,64,128]{2,1,0:T(8,128)(2,1)S(1)}, bf16[8,64,128]{2,1,0:T(8,128)(2,1)S(1)}, u32[]{:S(2)}, u32[]{:S(2)}) collective-permute-start(bf16[8,64,128]{2,1,0:T(8,128)(2,1)S(1)} %get-tuple-element.55.refs_2_.refs_3_), channel_id=1, source_target_pairs={{0,16},{8,24},{16,0},{24,8},{1,17},{9,25},{17,1},{25,9},{2,18},{10... | collective-permute-start | bytes 393224 | tf_op jit(solution)/shard_map/ppermute | solution.py:39
  38.6 2.5 %collective-permute-start.17 = (bf16[8,64,128]{2,1,0:T(8,128)(2,1)S(1)}, bf16[8,64,128]{2,1,0:T(8,128)(2,1)S(1)}, u32[]{:S(2)}, u32[]{:S(2)}) collective-permute-start(bf16[8,64,128]{2,1,0:T(8,128)(2,1)S(1)} %get-tuple-element.55.refs_2_.refs_3_), channel_id=1, source_target_pairs={{0,6},{1,7},{2,4},{3,5},{4,2},{5,3},{6,0},{7,1},{8,14},{9,15},{10,... | collective-permute-start | bytes 393224 | tf_op jit(solution)/shard_map/ppermute | solution.py:39
  42.4 1.7 %collective-permute-done.24.refs_5_ = bf16[7,64,128]{2,1,0:T(8,128)(2,1)S(1)} collective-permute-done((bf16[7,64,128]{2,1,0:T(8,128)(2,1)S(1)}, bf16[7,64,128]{2,1,0:T(8,128)(2,1)S(1)}, u32[]{:S(2)}, u32[]{:S(2)}) %collective-permute-start.24) | collective-permute-done | bytes 114720 | tf_op jit(solution)/shard_map/ppermute | solution.py:39
  44.2 1.3 %collective-permute-start.26 = (bf16[9,64,128]{2,1,0:T(8,128)(2,1)S(1)}, bf16[9,64,128]{2,1,0:T(8,128)(2,1)S(1)}, u32[]{:S(2)}, u32[]{:S(2)}) collective-permute-start(bf16[9,64,128]{2,1,0:T(8,128)(2,1)S(1)} %pad_maximum_fusion.1), channel_id=1, source_target_pairs={{0,8},{8,0},{16,24},{24,16},{1,9},{9,1},{17,25},{25,17},{2,10},{10... | collective-permute-start | bytes 442376 | tf_op jit(solution)/shard_map/ppermute | solution.py:39
  47.1 0.8 collective-permute-done.22.refs_8_
  48.1 1.1 %shard_map.67 = (f32[8,64,128]{2,1,0:T(8,128)S(1)}, f32[32,64,128]{2,1,0:T(8,128)S(1)}, bf16[512,128]{1,0:T(8,128)(2,1)S(1)}, bf16[512,128]{1,0:T(8,128)(2,1)S(1)}, bf16[512,128]{1,0:T(8,128)(2,1)S(1)}) custom-call(s32[3,32]{1,0:T(4,128)S(1)} %shard_map.59.refs_0_.refs_1_, bf16[32,128,128]{2,1,0:T(8,128)(2,1)S(1)} %bitcast.7, ...), custom_call_target="tpu_custom_call", output_to_operand_aliasing={{1}: (10, {})} | custom-call | flops 67108864 | bytes 3146112 | tf_op jit(solution)/shard_map/pallas_call | solution.py:25
  49.5 1.4 %shard_map.68 = (f32[64,64,128]{2,1,0:T(8,128)S(1)}, bf16[4,512,128]{2,1,0:T(8,128)(2,1)S(1)}) custom-call(f32[8,64,128]{2,1,0:T(8,128)S(1)} %get-tuple-element.57.refs_0_.refs_4_, s32[3,32]{1,0:T(4,128)S(1)} %shard_map.59.refs_0_.refs_1_, bf16[32,128,128]{2,1,0:T(8,128)(2,1)S(1)} %bitcast.8, ...), custom_call_target="tpu_custom_call", output_to_operand_aliasing={{0}: (7, {})} | custom-call | flops 67108864 | bytes 3670400 | tf_op jit(solution)/shard_map/pallas_call | solution.py:25
  51.1 2.0 %collective-permute-start.31 = (bf16[512,128]{1,0:T(8,128)(2,1)S(1)}, bf16[512,128]{1,0:T(8,128)(2,1)S(1)}, u32[]{:S(2)}, u32[]{:S(2)}) collective-permute-start(bf16[512,128]{1,0:T(8,128)(2,1)S(1)} %get-tuple-element.67), channel_id=1, source_target_pairs={{0,8},{8,0},{16,24},{24,16},{1,9},{9,1},{17,25},{25,17},{2,10},{10... | collective-permute-start | bytes 393224 | tf_op jit(solution)/shard_map/ppermute | solution.py:39
  53.6 1.9 %collective-permute-start.33 = (bf16[512,128]{1,0:T(8,128)(2,1)S(1)}, bf16[512,128]{1,0:T(8,128)(2,1)S(1)}, u32[]{:S(2)}, u32[]{:S(2)}) collective-permute-start(bf16[512,128]{1,0:T(8,128)(2,1)S(1)} %get-tuple-element.69), channel_id=1, source_target_pairs={{0,24},{8,16},{16,8},{24,0},{1,25},{9,17},{17,9},{25,1},{2,26},{10... | collective-permute-start | bytes 393224 | tf_op jit(solution)/shard_map/ppermute | solution.py:39
  55.6 2.4 %collective-permute-start.28 = (bf16[512,128]{1,0:T(8,128)(2,1)S(1)}, bf16[512,128]{1,0:T(8,128)(2,1)S(1)}, u32[]{:S(2)}, u32[]{:S(2)}) collective-permute-start(bf16[512,128]{1,0:T(8,128)(2,1)S(1)} %get-tuple-element.64), channel_id=1, source_target_pairs={{0,6},{1,7},{2,4},{3,5},{4,2},{5,3},{6,0},{7,1},{8,14},{9,15},{10,... | collective-permute-start | bytes 393224 | tf_op jit(solution)/shard_map/ppermute | solution.py:39
  58.6 1.5 %collective-permute-start.30 = (bf16[512,128]{1,0:T(8,128)(2,1)S(1)}, bf16[512,128]{1,0:T(8,128)(2,1)S(1)}, u32[]{:S(2)}, u32[]{:S(2)}) collective-permute-start(bf16[512,128]{1,0:T(8,128)(2,1)S(1)} %get-tuple-element.66), channel_id=1, source_target_pairs={{0,2},{1,3},{2,0},{3,1},{4,6},{5,7},{6,4},{7,5},{8,10},{9,11},{10,... | collective-permute-start | bytes 393224 | tf_op jit(solution)/shard_map/ppermute | solution.py:39
  60.2 5.8 %collective-permute-done.32.refs_9_ = bf16[512,128]{1,0:T(8,128)(2,1)S(1)} collective-permute-done((bf16[512,128]{1,0:T(8,128)(2,1)S(1)}, bf16[512,128]{1,0:T(8,128)(2,1)S(1)}, u32[]{:S(2)}, u32[]{:S(2)}) %collective-permute-start.32) | collective-permute-done | bytes 131104 | tf_op jit(solution)/shard_map/ppermute | solution.py:39
  66.2 2.5 %collective-permute-start.42 = (bf16[8,64,128]{2,1,0:T(8,128)(2,1)S(1)}, bf16[8,64,128]{2,1,0:T(8,128)(2,1)S(1)}, u32[]{:S(2)}, u32[]{:S(2)}) collective-permute-start(bf16[8,64,128]{2,1,0:T(8,128)(2,1)S(1)} %get-tuple-element.71.refs_2_.refs_3_), channel_id=1, source_target_pairs={{0,16},{8,24},{16,0},{24,8},{1,17},{9,25},{17,1},{25,9},{2,18},{10... | collective-permute-start | bytes 393224 | tf_op jit(solution)/shard_map/ppermute | solution.py:39
  68.9 1.8 %collective-permute-start.34 = (bf16[8,64,128]{2,1,0:T(8,128)(2,1)S(1)}, bf16[8,64,128]{2,1,0:T(8,128)(2,1)S(1)}, u32[]{:S(2)}, u32[]{:S(2)}) collective-permute-start(bf16[8,64,128]{2,1,0:T(8,128)(2,1)S(1)} %get-tuple-element.71.refs_2_.refs_3_), channel_id=1, source_target_pairs={{0,6},{1,7},{2,4},{3,5},{4,2},{5,3},{6,0},{7,1},{8,14},{9,15},{10,... | collective-permute-start | bytes 393224 | tf_op jit(solution)/shard_map/ppermute | solution.py:39
  70.6 1.1 %collective-permute-start.35 = (bf16[8,64,128]{2,1,0:T(8,128)(2,1)S(1)}, bf16[8,64,128]{2,1,0:T(8,128)(2,1)S(1)}, u32[]{:S(2)}, u32[]{:S(2)}) collective-permute-start(bf16[8,64,128]{2,1,0:T(8,128)(2,1)S(1)} %get-tuple-element.71.refs_2_.refs_3_), channel_id=1, source_target_pairs={{0,4},{1,5},{2,6},{3,7},{4,0},{5,1},{6,2},{7,3},{8,12},{9,13},{10,... | collective-permute-start | bytes 393224 | tf_op jit(solution)/shard_map/ppermute | solution.py:39
  73.1 1.5 %collective-permute-done.41.refs_5_ = bf16[7,64,128]{2,1,0:T(8,128)(2,1)S(1)} collective-permute-done((bf16[7,64,128]{2,1,0:T(8,128)(2,1)S(1)}, bf16[7,64,128]{2,1,0:T(8,128)(2,1)S(1)}, u32[]{:S(2)}, u32[]{:S(2)}) %collective-permute-start.41) | collective-permute-done | bytes 114720 | tf_op jit(solution)/shard_map/ppermute | solution.py:39
  74.9 1.0 collective-permute-start.43
  77.5 0.7 collective-permute-done.39.refs_8_
  78.4 1.0 %shard_map.71.refs_1_ = bf16[64,4096]{1,0:T(8,128)(2,1)S(1)} custom-call(s32[3,32]{1,0:T(4,128)S(1)} %shard_map.59.refs_0_.refs_1_, bf16[32,128,128]{2,1,0:T(8,128)(2,1)S(1)} %bitcast.9, bf16[8,64,128]{2,1,0:T(8,128)(2,1)S(1)} %get-tuple-element.71.refs_2_.refs_3_, bf16[8,64,128]{2,1,0:T(8,128)(2,1)S(1)} %collective-permute-done.34.refs_3_, ...), custom_call_target="tpu_custom_call" | custom-call | flops 67108864 | bytes 2097536 | tf_op jit(solution)/shard_map/pallas_call | solution.py:25
  79.4 0.7 collective-permute-done.43.refs_6_
  80.1 1.2 %shard_map.73 = f32[40,128]{1,0:T(8,128)S(1)} custom-call(s32[3,32]{1,0:T(4,128)S(1)} %shard_map.59.refs_0_.refs_1_, bf16[64,4096]{1,0:T(8,128)(2,1)S(1)} %shard_map.71.refs_1_, f32[64,128]{1,0:T(8,128)S(1)} %shard_map.72.refs_2_, bf16[8,64,128]{2,1,0:T(8,128)(2,1)S(1)} %get-tuple-element.71.refs_2_.refs_3_, ...), custom_call_target="tpu_custom_call" | custom-call | flops 33554432 | bytes 1081728 | tf_op jit(solution)/shard_map/pallas_call | solution.py:25
  81.4 1.2 %collective-permute-done.44 = f32[40,128]{1,0:T(8,128)S(1)} collective-permute-done((f32[40,128]{1,0:T(8,128)S(1)}, f32[40,128]{1,0:T(8,128)S(1)}, u32[]{:S(2)}, u32[]{:S(2)}) %collective-permute-start.44) | collective-permute-done | bytes 20512 | tf_op jit(solution)/shard_map/ppermute | solution.py:39
  82.6 1.1 %collective-permute-start.45 = (f32[40,128]{1,0:T(8,128)S(1)}, f32[40,128]{1,0:T(8,128)S(1)}, u32[]{:S(2)}, u32[]{:S(2)}) collective-permute-start(f32[40,128]{1,0:T(8,128)S(1)} %add.12), channel_id=1, source_target_pairs={{0,2},{1,3},{2,0},{3,1},{4,6},{5,7},{6,4},{7,5},{8,10},{9,11},{10,... | collective-permute-start | bytes 61448 | tf_op jit(solution)/shard_map/ppermute | solution.py:39
  83.7 0.8 collective-permute-start.46
  84.4 1.6 %collective-permute-start.47 = (f32[40,128]{1,0:T(8,128)S(1)}, f32[40,128]{1,0:T(8,128)S(1)}, u32[]{:S(2)}, u32[]{:S(2)}) collective-permute-start(f32[40,128]{1,0:T(8,128)S(1)} %add.12), channel_id=1, source_target_pairs={{0,6},{1,7},{2,4},{3,5},{4,2},{5,3},{6,0},{7,1},{8,14},{9,15},{10,... | collective-permute-start | bytes 61448 | tf_op jit(solution)/shard_map/ppermute | solution.py:39
  86.3 1.1 %collective-permute-done.46 = f32[40,128]{1,0:T(8,128)S(1)} collective-permute-done((f32[40,128]{1,0:T(8,128)S(1)}, f32[40,128]{1,0:T(8,128)S(1)}, u32[]{:S(2)}, u32[]{:S(2)}) %collective-permute-start.46) | collective-permute-done | bytes 20512 | tf_op jit(solution)/shard_map/ppermute | solution.py:39
  87.5 1.7 %collective-permute-done.47 = f32[40,128]{1,0:T(8,128)S(1)} collective-permute-done((f32[40,128]{1,0:T(8,128)S(1)}, f32[40,128]{1,0:T(8,128)S(1)}, u32[]{:S(2)}, u32[]{:S(2)}) %collective-permute-start.47) | collective-permute-done | bytes 20512 | tf_op jit(solution)/shard_map/ppermute | solution.py:39
  89.1 1.4 %collective-permute-start.48 = (f32[40,128]{1,0:T(8,128)S(1)}, f32[40,128]{1,0:T(8,128)S(1)}, u32[]{:S(2)}, u32[]{:S(2)}) collective-permute-start(f32[40,128]{1,0:T(8,128)S(1)} %add_add_fusion.refs_1_), channel_id=1, source_target_pairs={{0,8},{8,0},{16,24},{24,16},{1,9},{9,1},{17,25},{25,17},{2,10},{10... | collective-permute-start | bytes 61448 | tf_op jit(solution)/shard_map/ppermute | solution.py:39
  90.6 1.9 %collective-permute-start.49 = (f32[40,128]{1,0:T(8,128)S(1)}, f32[40,128]{1,0:T(8,128)S(1)}, u32[]{:S(2)}, u32[]{:S(2)}) collective-permute-start(f32[40,128]{1,0:T(8,128)S(1)} %add_add_fusion.refs_1_), channel_id=1, source_target_pairs={{0,16},{8,24},{16,0},{24,8},{1,17},{9,25},{17,1},{25,9},{2,18},{10... | collective-permute-start | bytes 61448 | tf_op jit(solution)/shard_map/ppermute | solution.py:39
  92.5 1.0 %collective-permute-start.50 = (f32[40,128]{1,0:T(8,128)S(1)}, f32[40,128]{1,0:T(8,128)S(1)}, u32[]{:S(2)}, u32[]{:S(2)}) collective-permute-start(f32[40,128]{1,0:T(8,128)S(1)} %add_add_fusion.refs_1_), channel_id=1, source_target_pairs={{0,24},{8,16},{16,8},{24,0},{1,25},{9,17},{17,9},{25,1},{2,26},{10... | collective-permute-start | bytes 61448 | tf_op jit(solution)/shard_map/ppermute | solution.py:39
  93.6 2.0 %collective-permute-done.49.refs_3_ = f32[40,128]{1,0:T(8,128)S(1)} collective-permute-done((f32[40,128]{1,0:T(8,128)S(1)}, f32[40,128]{1,0:T(8,128)S(1)}, u32[]{:S(2)}, u32[]{:S(2)}) %collective-permute-start.49) | collective-permute-done | bytes 20512 | tf_op jit(solution)/shard_map/ppermute | solution.py:39
  95.6 2.5 %collective-permute-done.50.refs_4_ = f32[40,128]{1,0:T(8,128)S(1)} collective-permute-done((f32[40,128]{1,0:T(8,128)S(1)}, f32[40,128]{1,0:T(8,128)S(1)}, u32[]{:S(2)}, u32[]{:S(2)}) %collective-permute-start.50) | collective-permute-done | bytes 20512 | tf_op jit(solution)/shard_map/ppermute | solution.py:39
  98.1 3.6 %shard_map.74 = (f32[64,1024]{1,0:T(8,128)}, f32[64,64]{1,0:T(8,128)}) custom-call(f32[64,1024]{1,0:T(8,128)S(1)} %get-tuple-element.70.refs_0_, f32[40,128]{1,0:T(8,128)S(1)} %add_add_fusion.refs_1_, f32[40,128]{1,0:T(8,128)S(1)} %collective-permute-done.48.refs_2_, f32[40,128]{1,0:T(8,128)S(1)} %collective-permute-done.49.refs_3_, ...), custom_call_target="tpu_custom_call" | custom-call | bytes 344064 | tf_op jit(solution)/shard_map/pallas_call | solution.py:25
  (94 shorter events, 15.3 us)
Async XLA Ops:
  1.6 11.5 %collective-permute-start.8 = (bf16[8,64,128]{2,1,0:T(8,128)(2,1)S(1)}, bf16[8,64,128]{2,1,0:T(8,128)(2,1)S(1)}, u32[]{:S(2)}, u32[]{:S(2)}) collective-permute-start(bf16[8,64,128]{2,1,0:T(8,128)(2,1)S(1)} %shard_map.60.refs_2_.refs_3_), channel_id=1, source_target_pairs={{0,16},{8,24},{16,0},{24,8},{1,17},{9,25},{17,1},{25,9},{2,18},{10... | collective-permute-start | bytes 393224 | tf_op jit(solution)/shard_map/ppermute | solution.py:39
  5.7 7.3 %collective-permute-start.7 = (bf16[7,64,128]{2,1,0:T(8,128)(2,1)S(1)}, bf16[7,64,128]{2,1,0:T(8,128)(2,1)S(1)}, u32[]{:S(2)}, u32[]{:S(2)}) collective-permute-start(bf16[7,64,128]{2,1,0:T(8,128)(2,1)S(1)} %slice.24), channel_id=1, source_target_pairs={{0,8},{8,0},{16,24},{24,16},{1,9},{9,1},{17,25},{25,17},{2,10},{10... | collective-permute-start | bytes 344072 | tf_op jit(solution)/shard_map/ppermute | solution.py:39
  7.4 6.6 %collective-permute-start = (bf16[8,64,128]{2,1,0:T(8,128)(2,1)S(1)}, bf16[8,64,128]{2,1,0:T(8,128)(2,1)S(1)}, u32[]{:S(2)}, u32[]{:S(2)}) collective-permute-start(bf16[8,64,128]{2,1,0:T(8,128)(2,1)S(1)} %shard_map.60.refs_2_.refs_3_), channel_id=1, source_target_pairs={{0,6},{1,7},{2,4},{3,5},{4,2},{5,3},{6,0},{7,1},{8,14},{9,15},{10,... | collective-permute-start | bytes 393224 | tf_op jit(solution)/shard_map/ppermute | solution.py:39
  9.8 5.9 %collective-permute-start.1 = (bf16[8,64,128]{2,1,0:T(8,128)(2,1)S(1)}, bf16[8,64,128]{2,1,0:T(8,128)(2,1)S(1)}, u32[]{:S(2)}, u32[]{:S(2)}) collective-permute-start(bf16[8,64,128]{2,1,0:T(8,128)(2,1)S(1)} %shard_map.60.refs_2_.refs_3_), channel_id=1, source_target_pairs={{0,4},{1,5},{2,6},{3,7},{4,0},{5,1},{6,2},{7,3},{8,12},{9,13},{10,... | collective-permute-start | bytes 393224 | tf_op jit(solution)/shard_map/ppermute | solution.py:39
  10.3 5.5 %collective-permute-start.2 = (bf16[8,64,128]{2,1,0:T(8,128)(2,1)S(1)}, bf16[8,64,128]{2,1,0:T(8,128)(2,1)S(1)}, u32[]{:S(2)}, u32[]{:S(2)}) collective-permute-start(bf16[8,64,128]{2,1,0:T(8,128)(2,1)S(1)} %shard_map.60.refs_2_.refs_3_), channel_id=1, source_target_pairs={{0,2},{1,3},{2,0},{3,1},{4,6},{5,7},{6,4},{7,5},{8,10},{9,11},{10,... | collective-permute-start | bytes 393224 | tf_op jit(solution)/shard_map/ppermute | solution.py:39
  13.1 6.6 %collective-permute-start.9 = (bf16[9,64,128]{2,1,0:T(8,128)(2,1)S(1)}, bf16[9,64,128]{2,1,0:T(8,128)(2,1)S(1)}, u32[]{:S(2)}, u32[]{:S(2)}) collective-permute-start(bf16[9,64,128]{2,1,0:T(8,128)(2,1)S(1)} %pad_maximum_fusion), channel_id=1, source_target_pairs={{0,8},{8,0},{16,24},{24,16},{1,9},{9,1},{17,25},{25,17},{2,10},{10... | collective-permute-start | bytes 442376 | tf_op jit(solution)/shard_map/ppermute | solution.py:39
  13.6 2.6 %collective-permute-start.3 = (bf16[8,64,128]{2,1,0:T(8,128)(2,1)S(1)}, bf16[8,64,128]{2,1,0:T(8,128)(2,1)S(1)}, u32[]{:S(2)}, u32[]{:S(2)}) collective-permute-start(bf16[8,64,128]{2,1,0:T(8,128)(2,1)S(1)} %shard_map.60.refs_2_.refs_3_), channel_id=1, source_target_pairs={{0,1},{1,0},{2,3},{3,2},{4,5},{5,4},{6,7},{7,6},{8,9},{9,8},{10,11... | collective-permute-start | bytes 393224 | tf_op jit(solution)/shard_map/ppermute | solution.py:39
  13.9 2.3 %collective-permute-start.4 = (bf16[8,64,128]{2,1,0:T(8,128)(2,1)S(1)}, bf16[8,64,128]{2,1,0:T(8,128)(2,1)S(1)}, u32[]{:S(2)}, u32[]{:S(2)}) collective-permute-start(bf16[8,64,128]{2,1,0:T(8,128)(2,1)S(1)} %collective-permute-done.refs_3_), channel_id=1, source_target_pairs={{0,1},{1,0},{2,3},{3,2},{4,5},{5,4},{6,7},{7,6},{8,9},{9,8},{10,11... | collective-permute-start | bytes 393224 | tf_op jit(solution)/shard_map/ppermute | solution.py:39
  15.7 1.3 %collective-permute-start.5 = (bf16[8,64,128]{2,1,0:T(8,128)(2,1)S(1)}, bf16[8,64,128]{2,1,0:T(8,128)(2,1)S(1)}, u32[]{:S(2)}, u32[]{:S(2)}) collective-permute-start(bf16[8,64,128]{2,1,0:T(8,128)(2,1)S(1)} %collective-permute-done.1.refs_4_), channel_id=1, source_target_pairs={{0,1},{1,0},{2,3},{3,2},{4,5},{5,4},{6,7},{7,6},{8,9},{9,8},{10,11... | collective-permute-start | bytes 393224 | tf_op jit(solution)/shard_map/ppermute | solution.py:39
  15.8 1.4 %collective-permute-start.6 = (bf16[8,64,128]{2,1,0:T(8,128)(2,1)S(1)}, bf16[8,64,128]{2,1,0:T(8,128)(2,1)S(1)}, u32[]{:S(2)}, u32[]{:S(2)}) collective-permute-start(bf16[8,64,128]{2,1,0:T(8,128)(2,1)S(1)} %collective-permute-done.2.refs_5_), channel_id=1, source_target_pairs={{0,1},{1,0},{2,3},{3,2},{4,5},{5,4},{6,7},{7,6},{8,9},{9,8},{10,11... | collective-permute-start | bytes 393224 | tf_op jit(solution)/shard_map/ppermute | solution.py:39
  21.3 4.8 %collective-permute-start.10 = (bf16[4,528,128]{2,1,0:T(8,128)(2,1)S(1)}, bf16[4,528,128]{2,1,0:T(8,128)(2,1)S(1)}, u32[]{:S(2)}, u32[]{:S(2)}) collective-permute-start(bf16[4,528,128]{2,1,0:T(8,128)(2,1)S(1)} %get-tuple-element.44), channel_id=1, source_target_pairs={{0,1},{1,0},{2,3},{3,2},{4,5},{5,4},{6,7},{7,6},{8,9},{9,8},{10,11... | collective-permute-start | bytes 1622024 | tf_op jit(solution)/shard_map/ppermute | solution.py:39
  21.7 7.8 %collective-permute-start.14 = (bf16[528,128]{1,0:T(8,128)(2,1)S(1)}, bf16[528,128]{1,0:T(8,128)(2,1)S(1)}, u32[]{:S(2)}, u32[]{:S(2)}) collective-permute-start(bf16[528,128]{1,0:T(8,128)(2,1)S(1)} %get-tuple-element.50), channel_id=1, source_target_pairs={{0,8},{8,0},{16,24},{24,16},{1,9},{9,1},{17,25},{25,17},{2,10},{10... | collective-permute-start | bytes 405512 | tf_op jit(solution)/shard_map/ppermute | solution.py:39
  22.1 13.2 %collective-permute-start.15 = (bf16[528,128]{1,0:T(8,128)(2,1)S(1)}, bf16[528,128]{1,0:T(8,128)(2,1)S(1)}, u32[]{:S(2)}, u32[]{:S(2)}) collective-permute-start(bf16[528,128]{1,0:T(8,128)(2,1)S(1)} %get-tuple-element.51), channel_id=1, source_target_pairs={{0,16},{8,24},{16,0},{24,8},{1,17},{9,25},{17,1},{25,9},{2,18},{10... | collective-permute-start | bytes 405512 | tf_op jit(solution)/shard_map/ppermute | solution.py:39
  23.6 11.7 %collective-permute-start.16 = (bf16[528,128]{1,0:T(8,128)(2,1)S(1)}, bf16[528,128]{1,0:T(8,128)(2,1)S(1)}, u32[]{:S(2)}, u32[]{:S(2)}) collective-permute-start(bf16[528,128]{1,0:T(8,128)(2,1)S(1)} %get-tuple-element.52), channel_id=1, source_target_pairs={{0,24},{8,16},{16,8},{24,0},{1,25},{9,17},{17,9},{25,1},{2,26},{10... | collective-permute-start | bytes 405512 | tf_op jit(solution)/shard_map/ppermute | solution.py:39
  26.2 9.1 %collective-permute-start.11 = (bf16[528,128]{1,0:T(8,128)(2,1)S(1)}, bf16[528,128]{1,0:T(8,128)(2,1)S(1)}, u32[]{:S(2)}, u32[]{:S(2)}) collective-permute-start(bf16[528,128]{1,0:T(8,128)(2,1)S(1)} %get-tuple-element.47), channel_id=1, source_target_pairs={{0,6},{1,7},{2,4},{3,5},{4,2},{5,3},{6,0},{7,1},{8,14},{9,15},{10,... | collective-permute-start | bytes 405512 | tf_op jit(solution)/shard_map/ppermute | solution.py:39
  28.0 7.3 %collective-permute-start.12 = (bf16[528,128]{1,0:T(8,128)(2,1)S(1)}, bf16[528,128]{1,0:T(8,128)(2,1)S(1)}, u32[]{:S(2)}, u32[]{:S(2)}) collective-permute-start(bf16[528,128]{1,0:T(8,128)(2,1)S(1)} %get-tuple-element.48), channel_id=1, source_target_pairs={{0,4},{1,5},{2,6},{3,7},{4,0},{5,1},{6,2},{7,3},{8,12},{9,13},{10,... | collective-permute-start | bytes 405512 | tf_op jit(solution)/shard_map/ppermute | solution.py:39
  29.4 5.9 %collective-permute-start.13 = (bf16[528,128]{1,0:T(8,128)(2,1)S(1)}, bf16[528,128]{1,0:T(8,128)(2,1)S(1)}, u32[]{:S(2)}, u32[]{:S(2)}) collective-permute-start(bf16[528,128]{1,0:T(8,128)(2,1)S(1)} %get-tuple-element.49), channel_id=1, source_target_pairs={{0,2},{1,3},{2,0},{3,1},{4,6},{5,7},{6,4},{7,5},{8,10},{9,11},{10,... | collective-permute-start | bytes 405512 | tf_op jit(solution)/shard_map/ppermute | solution.py:39
  35.5 8.7 %collective-permute-start.25 = (bf16[8,64,128]{2,1,0:T(8,128)(2,1)S(1)}, bf16[8,64,128]{2,1,0:T(8,128)(2,1)S(1)}, u32[]{:S(2)}, u32[]{:S(2)}) collective-permute-start(bf16[8,64,128]{2,1,0:T(8,128)(2,1)S(1)} %get-tuple-element.55.refs_2_.refs_3_), channel_id=1, source_target_pairs={{0,16},{8,24},{16,0},{24,8},{1,17},{9,25},{17,1},{25,9},{2,18},{10... | collective-permute-start | bytes 393224 | tf_op jit(solution)/shard_map/ppermute | solution.py:39
  38.5 5.5 %collective-permute-start.24 = (bf16[7,64,128]{2,1,0:T(8,128)(2,1)S(1)}, bf16[7,64,128]{2,1,0:T(8,128)(2,1)S(1)}, u32[]{:S(2)}, u32[]{:S(2)}) collective-permute-start(bf16[7,64,128]{2,1,0:T(8,128)(2,1)S(1)} %slice.20), channel_id=1, source_target_pairs={{0,8},{8,0},{16,24},{24,16},{1,9},{9,1},{17,25},{25,17},{2,10},{10... | collective-permute-start | bytes 344072 | tf_op jit(solution)/shard_map/ppermute | solution.py:39
  38.6 7.0 %collective-permute-start.17 = (bf16[8,64,128]{2,1,0:T(8,128)(2,1)S(1)}, bf16[8,64,128]{2,1,0:T(8,128)(2,1)S(1)}, u32[]{:S(2)}, u32[]{:S(2)}) collective-permute-start(bf16[8,64,128]{2,1,0:T(8,128)(2,1)S(1)} %get-tuple-element.55.refs_2_.refs_3_), channel_id=1, source_target_pairs={{0,6},{1,7},{2,4},{3,5},{4,2},{5,3},{6,0},{7,1},{8,14},{9,15},{10,... | collective-permute-start | bytes 393224 | tf_op jit(solution)/shard_map/ppermute | solution.py:39
  41.1 5.5 %collective-permute-start.18 = (bf16[8,64,128]{2,1,0:T(8,128)(2,1)S(1)}, bf16[8,64,128]{2,1,0:T(8,128)(2,1)S(1)}, u32[]{:S(2)}, u32[]{:S(2)}) collective-permute-start(bf16[8,64,128]{2,1,0:T(8,128)(2,1)S(1)} %get-tuple-element.55.refs_2_.refs_3_), channel_id=1, source_target_pairs={{0,4},{1,5},{2,6},{3,7},{4,0},{5,1},{6,2},{7,3},{8,12},{9,13},{10,... | collective-permute-start | bytes 393224 | tf_op jit(solution)/shard_map/ppermute | solution.py:39
  41.6 5.1 %collective-permute-start.19 = (bf16[8,64,128]{2,1,0:T(8,128)(2,1)S(1)}, bf16[8,64,128]{2,1,0:T(8,128)(2,1)S(1)}, u32[]{:S(2)}, u32[]{:S(2)}) collective-permute-start(bf16[8,64,128]{2,1,0:T(8,128)(2,1)S(1)} %get-tuple-element.55.refs_2_.refs_3_), channel_id=1, source_target_pairs={{0,2},{1,3},{2,0},{3,1},{4,6},{5,7},{6,4},{7,5},{8,10},{9,11},{10,... | collective-permute-start | bytes 393224 | tf_op jit(solution)/shard_map/ppermute | solution.py:39
  44.2 5.2 %collective-permute-start.26 = (bf16[9,64,128]{2,1,0:T(8,128)(2,1)S(1)}, bf16[9,64,128]{2,1,0:T(8,128)(2,1)S(1)}, u32[]{:S(2)}, u32[]{:S(2)}) collective-permute-start(bf16[9,64,128]{2,1,0:T(8,128)(2,1)S(1)} %pad_maximum_fusion.1), channel_id=1, source_target_pairs={{0,8},{8,0},{16,24},{24,16},{1,9},{9,1},{17,25},{25,17},{2,10},{10... | collective-permute-start | bytes 442376 | tf_op jit(solution)/shard_map/ppermute | solution.py:39
  45.6 1.6 %collective-permute-start.20 = (bf16[8,64,128]{2,1,0:T(8,128)(2,1)S(1)}, bf16[8,64,128]{2,1,0:T(8,128)(2,1)S(1)}, u32[]{:S(2)}, u32[]{:S(2)}) collective-permute-start(bf16[8,64,128]{2,1,0:T(8,128)(2,1)S(1)} %get-tuple-element.55.refs_2_.refs_3_), channel_id=1, source_target_pairs={{0,1},{1,0},{2,3},{3,2},{4,5},{5,4},{6,7},{7,6},{8,9},{9,8},{10,11... | collective-permute-start | bytes 393224 | tf_op jit(solution)/shard_map/ppermute | solution.py:39
  45.6 1.5 %collective-permute-start.21 = (bf16[8,64,128]{2,1,0:T(8,128)(2,1)S(1)}, bf16[8,64,128]{2,1,0:T(8,128)(2,1)S(1)}, u32[]{:S(2)}, u32[]{:S(2)}) collective-permute-start(bf16[8,64,128]{2,1,0:T(8,128)(2,1)S(1)} %collective-permute-done.17.refs_3_), channel_id=1, source_target_pairs={{0,1},{1,0},{2,3},{3,2},{4,5},{5,4},{6,7},{7,6},{8,9},{9,8},{10,11... | collective-permute-start | bytes 393224 | tf_op jit(solution)/shard_map/ppermute | solution.py:39
  46.6 1.3 %collective-permute-start.22 = (bf16[8,64,128]{2,1,0:T(8,128)(2,1)S(1)}, bf16[8,64,128]{2,1,0:T(8,128)(2,1)S(1)}, u32[]{:S(2)}, u32[]{:S(2)}) collective-permute-start(bf16[8,64,128]{2,1,0:T(8,128)(2,1)S(1)} %collective-permute-done.18.refs_4_), channel_id=1, source_target_pairs={{0,1},{1,0},{2,3},{3,2},{4,5},{5,4},{6,7},{7,6},{8,9},{9,8},{10,11... | collective-permute-start | bytes 393224 | tf_op jit(solution)/shard_map/ppermute | solution.py:39
  46.7 1.4 %collective-permute-start.23 = (bf16[8,64,128]{2,1,0:T(8,128)(2,1)S(1)}, bf16[8,64,128]{2,1,0:T(8,128)(2,1)S(1)}, u32[]{:S(2)}, u32[]{:S(2)}) collective-permute-start(bf16[8,64,128]{2,1,0:T(8,128)(2,1)S(1)} %collective-permute-done.19.refs_5_), channel_id=1, source_target_pairs={{0,1},{1,0},{2,3},{3,2},{4,5},{5,4},{6,7},{7,6},{8,9},{9,8},{10,11... | collective-permute-start | bytes 393224 | tf_op jit(solution)/shard_map/ppermute | solution.py:39
  50.9 4.6 %collective-permute-start.27 = (bf16[4,512,128]{2,1,0:T(8,128)(2,1)S(1)}, bf16[4,512,128]{2,1,0:T(8,128)(2,1)S(1)}, u32[]{:S(2)}, u32[]{:S(2)}) collective-permute-start(bf16[4,512,128]{2,1,0:T(8,128)(2,1)S(1)} %get-tuple-element.62), channel_id=1, source_target_pairs={{0,1},{1,0},{2,3},{3,2},{4,5},{5,4},{6,7},{7,6},{8,9},{9,8},{10,11... | collective-permute-start | bytes 1572872 | tf_op jit(solution)/shard_map/ppermute | solution.py:39
  51.1 7.6 %collective-permute-start.31 = (bf16[512,128]{1,0:T(8,128)(2,1)S(1)}, bf16[512,128]{1,0:T(8,128)(2,1)S(1)}, u32[]{:S(2)}, u32[]{:S(2)}) collective-permute-start(bf16[512,128]{1,0:T(8,128)(2,1)S(1)} %get-tuple-element.67), channel_id=1, source_target_pairs={{0,8},{8,0},{16,24},{24,16},{1,9},{9,1},{17,25},{25,17},{2,10},{10... | collective-permute-start | bytes 393224 | tf_op jit(solution)/shard_map/ppermute | solution.py:39
  53.1 12.9 %collective-permute-start.32 = (bf16[512,128]{1,0:T(8,128)(2,1)S(1)}, bf16[512,128]{1,0:T(8,128)(2,1)S(1)}, u32[]{:S(2)}, u32[]{:S(2)}) collective-permute-start(bf16[512,128]{1,0:T(8,128)(2,1)S(1)} %get-tuple-element.68), channel_id=1, source_target_pairs={{0,16},{8,24},{16,0},{24,8},{1,17},{9,25},{17,1},{25,9},{2,18},{10... | collective-permute-start | bytes 393224 | tf_op jit(solution)/shard_map/ppermute | solution.py:39
  53.6 12.4 %collective-permute-start.33 = (bf16[512,128]{1,0:T(8,128)(2,1)S(1)}, bf16[512,128]{1,0:T(8,128)(2,1)S(1)}, u32[]{:S(2)}, u32[]{:S(2)}) collective-permute-start(bf16[512,128]{1,0:T(8,128)(2,1)S(1)} %get-tuple-element.69), channel_id=1, source_target_pairs={{0,24},{8,16},{16,8},{24,0},{1,25},{9,17},{17,9},{25,1},{2,26},{10... | collective-permute-start | bytes 393224 | tf_op jit(solution)/shard_map/ppermute | solution.py:39
  55.6 10.4 %collective-permute-start.28 = (bf16[512,128]{1,0:T(8,128)(2,1)S(1)}, bf16[512,128]{1,0:T(8,128)(2,1)S(1)}, u32[]{:S(2)}, u32[]{:S(2)}) collective-permute-start(bf16[512,128]{1,0:T(8,128)(2,1)S(1)} %get-tuple-element.64), channel_id=1, source_target_pairs={{0,6},{1,7},{2,4},{3,5},{4,2},{5,3},{6,0},{7,1},{8,14},{9,15},{10,... | collective-permute-start | bytes 393224 | tf_op jit(solution)/shard_map/ppermute | solution.py:39
  58.1 8.0 %collective-permute-start.29 = (bf16[512,128]{1,0:T(8,128)(2,1)S(1)}, bf16[512,128]{1,0:T(8,128)(2,1)S(1)}, u32[]{:S(2)}, u32[]{:S(2)}) collective-permute-start(bf16[512,128]{1,0:T(8,128)(2,1)S(1)} %get-tuple-element.65), channel_id=1, source_target_pairs={{0,4},{1,5},{2,6},{3,7},{4,0},{5,1},{6,2},{7,3},{8,12},{9,13},{10,... | collective-permute-start | bytes 393224 | tf_op jit(solution)/shard_map/ppermute | solution.py:39
  58.6 7.4 %collective-permute-start.30 = (bf16[512,128]{1,0:T(8,128)(2,1)S(1)}, bf16[512,128]{1,0:T(8,128)(2,1)S(1)}, u32[]{:S(2)}, u32[]{:S(2)}) collective-permute-start(bf16[512,128]{1,0:T(8,128)(2,1)S(1)} %get-tuple-element.66), channel_id=1, source_target_pairs={{0,2},{1,3},{2,0},{3,1},{4,6},{5,7},{6,4},{7,5},{8,10},{9,11},{10,... | collective-permute-start | bytes 393224 | tf_op jit(solution)/shard_map/ppermute | solution.py:39
  66.2 8.6 %collective-permute-start.42 = (bf16[8,64,128]{2,1,0:T(8,128)(2,1)S(1)}, bf16[8,64,128]{2,1,0:T(8,128)(2,1)S(1)}, u32[]{:S(2)}, u32[]{:S(2)}) collective-permute-start(bf16[8,64,128]{2,1,0:T(8,128)(2,1)S(1)} %get-tuple-element.71.refs_2_.refs_3_), channel_id=1, source_target_pairs={{0,16},{8,24},{16,0},{24,8},{1,17},{9,25},{17,1},{25,9},{2,18},{10... | collective-permute-start | bytes 393224 | tf_op jit(solution)/shard_map/ppermute | solution.py:39
  68.8 5.8 %collective-permute-start.41 = (bf16[7,64,128]{2,1,0:T(8,128)(2,1)S(1)}, bf16[7,64,128]{2,1,0:T(8,128)(2,1)S(1)}, u32[]{:S(2)}, u32[]{:S(2)}) collective-permute-start(bf16[7,64,128]{2,1,0:T(8,128)(2,1)S(1)} %slice.22), channel_id=1, source_target_pairs={{0,8},{8,0},{16,24},{24,16},{1,9},{9,1},{17,25},{25,17},{2,10},{10... | collective-permute-start | bytes 344072 | tf_op jit(solution)/shard_map/ppermute | solution.py:39
  68.9 7.2 %collective-permute-start.34 = (bf16[8,64,128]{2,1,0:T(8,128)(2,1)S(1)}, bf16[8,64,128]{2,1,0:T(8,128)(2,1)S(1)}, u32[]{:S(2)}, u32[]{:S(2)}) collective-permute-start(bf16[8,64,128]{2,1,0:T(8,128)(2,1)S(1)} %get-tuple-element.71.refs_2_.refs_3_), channel_id=1, source_target_pairs={{0,6},{1,7},{2,4},{3,5},{4,2},{5,3},{6,0},{7,1},{8,14},{9,15},{10,... | collective-permute-start | bytes 393224 | tf_op jit(solution)/shard_map/ppermute | solution.py:39
  70.6 6.2 %collective-permute-start.35 = (bf16[8,64,128]{2,1,0:T(8,128)(2,1)S(1)}, bf16[8,64,128]{2,1,0:T(8,128)(2,1)S(1)}, u32[]{:S(2)}, u32[]{:S(2)}) collective-permute-start(bf16[8,64,128]{2,1,0:T(8,128)(2,1)S(1)} %get-tuple-element.71.refs_2_.refs_3_), channel_id=1, source_target_pairs={{0,4},{1,5},{2,6},{3,7},{4,0},{5,1},{6,2},{7,3},{8,12},{9,13},{10,... | collective-permute-start | bytes 393224 | tf_op jit(solution)/shard_map/ppermute | solution.py:39
  71.8 5.1 %collective-permute-start.36 = (bf16[8,64,128]{2,1,0:T(8,128)(2,1)S(1)}, bf16[8,64,128]{2,1,0:T(8,128)(2,1)S(1)}, u32[]{:S(2)}, u32[]{:S(2)}) collective-permute-start(bf16[8,64,128]{2,1,0:T(8,128)(2,1)S(1)} %get-tuple-element.71.refs_2_.refs_3_), channel_id=1, source_target_pairs={{0,2},{1,3},{2,0},{3,1},{4,6},{5,7},{6,4},{7,5},{8,10},{9,11},{10,... | collective-permute-start | bytes 393224 | tf_op jit(solution)/shard_map/ppermute | solution.py:39
  74.9 5.2 %collective-permute-start.43 = (bf16[9,64,128]{2,1,0:T(8,128)(2,1)S(1)}, bf16[9,64,128]{2,1,0:T(8,128)(2,1)S(1)}, u32[]{:S(2)}, u32[]{:S(2)}) collective-permute-start(bf16[9,64,128]{2,1,0:T(8,128)(2,1)S(1)} %pad_maximum_fusion.2), channel_id=1, source_target_pairs={{0,8},{8,0},{16,24},{24,16},{1,9},{9,1},{17,25},{25,17},{2,10},{10... | collective-permute-start | bytes 442376 | tf_op jit(solution)/shard_map/ppermute | solution.py:39
  75.9 1.5 %collective-permute-start.37 = (bf16[8,64,128]{2,1,0:T(8,128)(2,1)S(1)}, bf16[8,64,128]{2,1,0:T(8,128)(2,1)S(1)}, u32[]{:S(2)}, u32[]{:S(2)}) collective-permute-start(bf16[8,64,128]{2,1,0:T(8,128)(2,1)S(1)} %get-tuple-element.71.refs_2_.refs_3_), channel_id=1, source_target_pairs={{0,1},{1,0},{2,3},{3,2},{4,5},{5,4},{6,7},{7,6},{8,9},{9,8},{10,11... | collective-permute-start | bytes 393224 | tf_op jit(solution)/shard_map/ppermute | solution.py:39
  76.9 1.5 %collective-permute-start.40 = (bf16[8,64,128]{2,1,0:T(8,128)(2,1)S(1)}, bf16[8,64,128]{2,1,0:T(8,128)(2,1)S(1)}, u32[]{:S(2)}, u32[]{:S(2)}) collective-permute-start(bf16[8,64,128]{2,1,0:T(8,128)(2,1)S(1)} %collective-permute-done.36.refs_5_), channel_id=1, source_target_pairs={{0,1},{1,0},{2,3},{3,2},{4,5},{5,4},{6,7},{7,6},{8,9},{9,8},{10,11... | collective-permute-start | bytes 393224 | tf_op jit(solution)/shard_map/ppermute | solution.py:39
  82.6 3.8 %collective-permute-start.45 = (f32[40,128]{1,0:T(8,128)S(1)}, f32[40,128]{1,0:T(8,128)S(1)}, u32[]{:S(2)}, u32[]{:S(2)}) collective-permute-start(f32[40,128]{1,0:T(8,128)S(1)} %add.12), channel_id=1, source_target_pairs={{0,2},{1,3},{2,0},{3,1},{4,6},{5,7},{6,4},{7,5},{8,10},{9,11},{10,... | collective-permute-start | bytes 61448 | tf_op jit(solution)/shard_map/ppermute | solution.py:39
  83.7 3.8 %collective-permute-start.46 = (f32[40,128]{1,0:T(8,128)S(1)}, f32[40,128]{1,0:T(8,128)S(1)}, u32[]{:S(2)}, u32[]{:S(2)}) collective-permute-start(f32[40,128]{1,0:T(8,128)S(1)} %add.12), channel_id=1, source_target_pairs={{0,4},{1,5},{2,6},{3,7},{4,0},{5,1},{6,2},{7,3},{8,12},{9,13},{10,... | collective-permute-start | bytes 61448 | tf_op jit(solution)/shard_map/ppermute | solution.py:39
  84.4 4.7 %collective-permute-start.47 = (f32[40,128]{1,0:T(8,128)S(1)}, f32[40,128]{1,0:T(8,128)S(1)}, u32[]{:S(2)}, u32[]{:S(2)}) collective-permute-start(f32[40,128]{1,0:T(8,128)S(1)} %add.12), channel_id=1, source_target_pairs={{0,6},{1,7},{2,4},{3,5},{4,2},{5,3},{6,0},{7,1},{8,14},{9,15},{10,... | collective-permute-start | bytes 61448 | tf_op jit(solution)/shard_map/ppermute | solution.py:39
  89.1 4.5 %collective-permute-start.48 = (f32[40,128]{1,0:T(8,128)S(1)}, f32[40,128]{1,0:T(8,128)S(1)}, u32[]{:S(2)}, u32[]{:S(2)}) collective-permute-start(f32[40,128]{1,0:T(8,128)S(1)} %add_add_fusion.refs_1_), channel_id=1, source_target_pairs={{0,8},{8,0},{16,24},{24,16},{1,9},{9,1},{17,25},{25,17},{2,10},{10... | collective-permute-start | bytes 61448 | tf_op jit(solution)/shard_map/ppermute | solution.py:39
  90.6 5.0 %collective-permute-start.49 = (f32[40,128]{1,0:T(8,128)S(1)}, f32[40,128]{1,0:T(8,128)S(1)}, u32[]{:S(2)}, u32[]{:S(2)}) collective-permute-start(f32[40,128]{1,0:T(8,128)S(1)} %add_add_fusion.refs_1_), channel_id=1, source_target_pairs={{0,16},{8,24},{16,0},{24,8},{1,17},{9,25},{17,1},{25,9},{2,18},{10... | collective-permute-start | bytes 61448 | tf_op jit(solution)/shard_map/ppermute | solution.py:39
  92.5 5.6 %collective-permute-start.50 = (f32[40,128]{1,0:T(8,128)S(1)}, f32[40,128]{1,0:T(8,128)S(1)}, u32[]{:S(2)}, u32[]{:S(2)}) collective-permute-start(f32[40,128]{1,0:T(8,128)S(1)} %add_add_fusion.refs_1_), channel_id=1, source_target_pairs={{0,24},{8,16},{16,8},{24,0},{1,25},{9,17},{17,9},{25,1},{2,26},{10... | collective-permute-start | bytes 61448 | tf_op jit(solution)/shard_map/ppermute | solution.py:39
  (9 other events, 22.7 us)

commit v17 on v16

--- a/solution.py
+++ b/solution.py
@@ -331,7 +331,8 @@
 
 
 def last_kernel(total_nodes, filtered_ref, *refs):
-    parts, (ritz_ref, rayleigh_ref) = refs[:-2], refs[-2:]
+    (own, *parts), (ritz_ref, rayleigh_ref) = refs[:-2], refs[-2:]
+    parts = [own, *parts[::-1]]
     n = filtered_ref.shape[0]
     half = n // 2
     sums = tree_sum([part[...] for part in parts]) * (1.0 / total_nodes)
@@ -344,14 +345,13 @@
     projected = lower + lower.T + jnp.where(row == col, diagonal, 0.0)
     inverse = inverse_factor(gram)
 
-    def dot(a, b, dims, precision=HIGHEST):
-        return lax.dot_general(a, b, dims, precision=precision, preferred_element_type=F32)
+    def dot(a, b, dims):
+        return lax.dot_general(a, b, dims, precision=HIGHEST, preferred_element_type=F32)
 
     half_way = dot(inverse, projected, NN)
     rayleigh_ref[...] = dot(half_way, inverse, NT)
     turned = dot(inverse, half_way, NT)
-    block = dot(inverse, filtered_ref[...], NN, lax.Precision.HIGH)
-    ritz_ref[...] = dot(turned, block, NN, lax.Precision.HIGH)
+    ritz_ref[...] = dot(turned, dot(inverse, filtered_ref[...], NN), NN)
 
 
 def tree_sum(parts):
@@ -470,13 +470,13 @@
         1,
     )
     sums = sums + trade(sums, "col", 1)
-    sums = tree_sum([sums, *exchange([sums] * (chips_n - 1), "col", 2)])
+    sums = tree_sum([*exchange([sums] * (chips_n - 1), "col", 2)[::-1], sums])
     return call(
         functools.partial(last_kernel, total_nodes),
         [vector_shape, jax.ShapeDtypeStruct((vectors_n, vectors_n), F32)],
         [],
         24,
-        [filtered, sums, *exchange([sums] * (rows_n - 1), "row")],
+        [filtered, sums, *exchange([sums] * (rows_n - 1), "row")[::-1]],
     )
 
 

time: 102 us -> 99.7 us (0.977)
  waiting for transfers between devices: 30.2 us -> 27.7 us
    ppermute x51, waiting for transfers between devices: 30.2 us -> 27.7 us  [trade(): return lax.ppermute(part, axis, [(i, i ^ d) for i in range(n)])]
where the time goes in v17:
time: 99.7 us; the launch traced here: 99.5 us
  starting transfers between devices  53.6 us (54%)
  waiting for transfers between devices  27.7 us (28%)
  Pallas kernels  13.6 us (14%)
  local copies, waits for them, and re-layouts  3.52 us (4%)
    ppermute x51, starting transfers between devices, trade(): return lax.ppermute(part, axis, [(i, i ^ d) for i in range(n)])  53.6 us
    ppermute x51, waiting for transfers between devices, trade(): return lax.ppermute(part, axis, [(i, i ^ d) for i in range(n)])  27.7 us
    pallas_call x16, Pallas kernels, call(): pl.pallas_call(lambda *refs: kernel(*refs[len(after):]), out_shape=jax.tr...  13.6 us
    unnamed x12, local copies, waits for them, and re-layouts  3.49 us
  transfers between devices with their start and end apart: 51, of which 30 were waited for; matrix products, arithmetic and copies ran while one was open for 0% of the time, Pallas kernels for 5%

profile of v17, /device:TPU:0, one launch (start us, length us, event | category | flops | bytes accessed | tf_op | source)
XLA Modules:
  0.0 99.5 jit_solution(10160173801776689111)
XLA Ops:
  0.6 0.9 copy-done.2
  1.6 4.1 %collective-permute-start.8 = (bf16[8,64,128]{2,1,0:T(8,128)(2,1)S(1)}, bf16[8,64,128]{2,1,0:T(8,128)(2,1)S(1)}, u32[]{:S(2)}, u32[]{:S(2)}) collective-permute-start(bf16[8,64,128]{2,1,0:T(8,128)(2,1)S(1)} %shard_map.60.refs_2_.refs_3_), channel_id=1, source_target_pairs={{0,16},{8,24},{16,0},{24,8},{1,17},{9,25},{17,1},{25,9},{2,18},{10... | collective-permute-start | bytes 393224 | tf_op jit(solution)/shard_map/ppermute | solution.py:39
  5.7 1.6 %collective-permute-start.7 = (bf16[7,64,128]{2,1,0:T(8,128)(2,1)S(1)}, bf16[7,64,128]{2,1,0:T(8,128)(2,1)S(1)}, u32[]{:S(2)}, u32[]{:S(2)}) collective-permute-start(bf16[7,64,128]{2,1,0:T(8,128)(2,1)S(1)} %slice.24), channel_id=1, source_target_pairs={{0,8},{8,0},{16,24},{24,16},{1,9},{9,1},{17,25},{25,17},{2,10},{10... | collective-permute-start | bytes 344072 | tf_op jit(solution)/shard_map/ppermute | solution.py:39
  7.4 2.4 %collective-permute-start = (bf16[8,64,128]{2,1,0:T(8,128)(2,1)S(1)}, bf16[8,64,128]{2,1,0:T(8,128)(2,1)S(1)}, u32[]{:S(2)}, u32[]{:S(2)}) collective-permute-start(bf16[8,64,128]{2,1,0:T(8,128)(2,1)S(1)} %shard_map.60.refs_2_.refs_3_), channel_id=1, source_target_pairs={{0,6},{1,7},{2,4},{3,5},{4,2},{5,3},{6,0},{7,1},{8,14},{9,15},{10,... | collective-permute-start | bytes 393224 | tf_op jit(solution)/shard_map/ppermute | solution.py:39
  14.1 1.6 %collective-permute-done.1.refs_4_ = bf16[8,64,128]{2,1,0:T(8,128)(2,1)S(1)} collective-permute-done((bf16[8,64,128]{2,1,0:T(8,128)(2,1)S(1)}, bf16[8,64,128]{2,1,0:T(8,128)(2,1)S(1)}, u32[]{:S(2)}, u32[]{:S(2)}) %collective-permute-start.1) | collective-permute-done | bytes 131104 | tf_op jit(solution)/shard_map/ppermute | solution.py:39
  16.3 0.8 collective-permute-done.5.refs_8_
  17.3 1.2 %copy-done = bf16[1,1,32,128,128]{4,3,2,1,0:T(8,128)(2,1)S(1)} copy-done((bf16[1,1,32,128,128]{4,3,2,1,0:T(8,128)(2,1)S(1)}, bf16[1,1,32,128,128]{4,3,2,1,0:T(8,128)(2,1)}, u32[]{:S(2)}) %copy-start) | copy-done | bytes 1048600
  18.5 1.2 %shard_map.62 = (f32[8,80,128]{2,1,0:T(8,128)S(1)}, f32[32,80,128]{2,1,0:T(8,128)S(1)}, bf16[528,128]{1,0:T(8,128)(2,1)S(1)}, bf16[528,128]{1,0:T(8,128)(2,1)S(1)}, bf16[528,128]{1,0:T(8,128)(2,1)S(1)}) custom-call(s32[3,32]{1,0:T(4,128)S(1)} %shard_map.59.refs_0_.refs_1_, bf16[32,128,128]{2,1,0:T(8,128)(2,1)S(1)} %bitcast.5, ...), custom_call_target="tpu_custom_call", output_to_operand_aliasing={{1}: (10, {})} | custom-call | flops 67108864 | bytes 3408256 | tf_op jit(solution)/shard_map/pallas_call | solution.py:25
  19.8 1.5 %shard_map.63 = (f32[64,80,128]{2,1,0:T(8,128)S(1)}, bf16[4,528,128]{2,1,0:T(8,128)(2,1)S(1)}) custom-call(f32[8,80,128]{2,1,0:T(8,128)S(1)} %get-tuple-element.39.refs_0_.refs_3_, s32[3,32]{1,0:T(4,128)S(1)} %shard_map.59.refs_0_.refs_1_, bf16[32,128,128]{2,1,0:T(8,128)(2,1)S(1)} %bitcast.6, ...), custom_call_target="tpu_custom_call", output_to_operand_aliasing={{0}: (7, {})} | custom-call | flops 67108864 | bytes 4194688 | tf_op jit(solution)/shard_map/pallas_call | solution.py:25
  22.1 1.5 %collective-permute-start.15 = (bf16[528,128]{1,0:T(8,128)(2,1)S(1)}, bf16[528,128]{1,0:T(8,128)(2,1)S(1)}, u32[]{:S(2)}, u32[]{:S(2)}) collective-permute-start(bf16[528,128]{1,0:T(8,128)(2,1)S(1)} %get-tuple-element.51), channel_id=1, source_target_pairs={{0,16},{8,24},{16,0},{24,8},{1,17},{9,25},{17,1},{25,9},{2,18},{10... | collective-permute-start | bytes 405512 | tf_op jit(solution)/shard_map/ppermute | solution.py:39
  23.6 2.4 %collective-permute-start.16 = (bf16[528,128]{1,0:T(8,128)(2,1)S(1)}, bf16[528,128]{1,0:T(8,128)(2,1)S(1)}, u32[]{:S(2)}, u32[]{:S(2)}) collective-permute-start(bf16[528,128]{1,0:T(8,128)(2,1)S(1)} %get-tuple-element.52), channel_id=1, source_target_pairs={{0,24},{8,16},{16,8},{24,0},{1,25},{9,17},{17,9},{25,1},{2,26},{10... | collective-permute-start | bytes 405512 | tf_op jit(solution)/shard_map/ppermute | solution.py:39
  26.2 1.8 %collective-permute-start.11 = (bf16[528,128]{1,0:T(8,128)(2,1)S(1)}, bf16[528,128]{1,0:T(8,128)(2,1)S(1)}, u32[]{:S(2)}, u32[]{:S(2)}) collective-permute-start(bf16[528,128]{1,0:T(8,128)(2,1)S(1)} %get-tuple-element.47), channel_id=1, source_target_pairs={{0,6},{1,7},{2,4},{3,5},{4,2},{5,3},{6,0},{7,1},{8,14},{9,15},{10,... | collective-permute-start | bytes 405512 | tf_op jit(solution)/shard_map/ppermute | solution.py:39
  28.0 1.2 %collective-permute-start.12 = (bf16[528,128]{1,0:T(8,128)(2,1)S(1)}, bf16[528,128]{1,0:T(8,128)(2,1)S(1)}, u32[]{:S(2)}, u32[]{:S(2)}) collective-permute-start(bf16[528,128]{1,0:T(8,128)(2,1)S(1)} %get-tuple-element.48), channel_id=1, source_target_pairs={{0,4},{1,5},{2,6},{3,7},{4,0},{5,1},{6,2},{7,3},{8,12},{9,13},{10,... | collective-permute-start | bytes 405512 | tf_op jit(solution)/shard_map/ppermute | solution.py:39
  29.4 1.5 %collective-permute-start.13 = (bf16[528,128]{1,0:T(8,128)(2,1)S(1)}, bf16[528,128]{1,0:T(8,128)(2,1)S(1)}, u32[]{:S(2)}, u32[]{:S(2)}) collective-permute-start(bf16[528,128]{1,0:T(8,128)(2,1)S(1)} %get-tuple-element.49), channel_id=1, source_target_pairs={{0,2},{1,3},{2,0},{3,1},{4,6},{5,7},{6,4},{7,5},{8,10},{9,11},{10,... | collective-permute-start | bytes 405512 | tf_op jit(solution)/shard_map/ppermute | solution.py:39
  30.9 4.4 %collective-permute-done.15.refs_8_ = bf16[528,128]{1,0:T(8,128)(2,1)S(1)} collective-permute-done((bf16[528,128]{1,0:T(8,128)(2,1)S(1)}, bf16[528,128]{1,0:T(8,128)(2,1)S(1)}, u32[]{:S(2)}, u32[]{:S(2)}) %collective-permute-start.15) | collective-permute-done | bytes 135200 | tf_op jit(solution)/shard_map/ppermute | solution.py:39
  35.5 3.0 %collective-permute-start.25 = (bf16[8,64,128]{2,1,0:T(8,128)(2,1)S(1)}, bf16[8,64,128]{2,1,0:T(8,128)(2,1)S(1)}, u32[]{:S(2)}, u32[]{:S(2)}) collective-permute-start(bf16[8,64,128]{2,1,0:T(8,128)(2,1)S(1)} %get-tuple-element.55.refs_2_.refs_3_), channel_id=1, source_target_pairs={{0,16},{8,24},{16,0},{24,8},{1,17},{9,25},{17,1},{25,9},{2,18},{10... | collective-permute-start | bytes 393224 | tf_op jit(solution)/shard_map/ppermute | solution.py:39
  38.6 2.5 %collective-permute-start.17 = (bf16[8,64,128]{2,1,0:T(8,128)(2,1)S(1)}, bf16[8,64,128]{2,1,0:T(8,128)(2,1)S(1)}, u32[]{:S(2)}, u32[]{:S(2)}) collective-permute-start(bf16[8,64,128]{2,1,0:T(8,128)(2,1)S(1)} %get-tuple-element.55.refs_2_.refs_3_), channel_id=1, source_target_pairs={{0,6},{1,7},{2,4},{3,5},{4,2},{5,3},{6,0},{7,1},{8,14},{9,15},{10,... | collective-permute-start | bytes 393224 | tf_op jit(solution)/shard_map/ppermute | solution.py:39
  42.4 1.7 %collective-permute-done.24.refs_5_ = bf16[7,64,128]{2,1,0:T(8,128)(2,1)S(1)} collective-permute-done((bf16[7,64,128]{2,1,0:T(8,128)(2,1)S(1)}, bf16[7,64,128]{2,1,0:T(8,128)(2,1)S(1)}, u32[]{:S(2)}, u32[]{:S(2)}) %collective-permute-start.24) | collective-permute-done | bytes 114720 | tf_op jit(solution)/shard_map/ppermute | solution.py:39
  44.2 1.3 %collective-permute-start.26 = (bf16[9,64,128]{2,1,0:T(8,128)(2,1)S(1)}, bf16[9,64,128]{2,1,0:T(8,128)(2,1)S(1)}, u32[]{:S(2)}, u32[]{:S(2)}) collective-permute-start(bf16[9,64,128]{2,1,0:T(8,128)(2,1)S(1)} %pad_maximum_fusion.1), channel_id=1, source_target_pairs={{0,8},{8,0},{16,24},{24,16},{1,9},{9,1},{17,25},{25,17},{2,10},{10... | collective-permute-start | bytes 442376 | tf_op jit(solution)/shard_map/ppermute | solution.py:39
  47.1 0.8 collective-permute-done.22.refs_8_
  48.1 1.1 %shard_map.67 = (f32[8,64,128]{2,1,0:T(8,128)S(1)}, f32[32,64,128]{2,1,0:T(8,128)S(1)}, bf16[512,128]{1,0:T(8,128)(2,1)S(1)}, bf16[512,128]{1,0:T(8,128)(2,1)S(1)}, bf16[512,128]{1,0:T(8,128)(2,1)S(1)}) custom-call(s32[3,32]{1,0:T(4,128)S(1)} %shard_map.59.refs_0_.refs_1_, bf16[32,128,128]{2,1,0:T(8,128)(2,1)S(1)} %bitcast.7, ...), custom_call_target="tpu_custom_call", output_to_operand_aliasing={{1}: (10, {})} | custom-call | flops 67108864 | bytes 3146112 | tf_op jit(solution)/shard_map/pallas_call | solution.py:25
  49.4 1.4 %shard_map.68 = (f32[64,64,128]{2,1,0:T(8,128)S(1)}, bf16[4,512,128]{2,1,0:T(8,128)(2,1)S(1)}) custom-call(f32[8,64,128]{2,1,0:T(8,128)S(1)} %get-tuple-element.57.refs_0_.refs_4_, s32[3,32]{1,0:T(4,128)S(1)} %shard_map.59.refs_0_.refs_1_, bf16[32,128,128]{2,1,0:T(8,128)(2,1)S(1)} %bitcast.8, ...), custom_call_target="tpu_custom_call", output_to_operand_aliasing={{0}: (7, {})} | custom-call | flops 67108864 | bytes 3670400 | tf_op jit(solution)/shard_map/pallas_call | solution.py:25
  51.1 2.0 %collective-permute-start.31 = (bf16[512,128]{1,0:T(8,128)(2,1)S(1)}, bf16[512,128]{1,0:T(8,128)(2,1)S(1)}, u32[]{:S(2)}, u32[]{:S(2)}) collective-permute-start(bf16[512,128]{1,0:T(8,128)(2,1)S(1)} %get-tuple-element.67), channel_id=1, source_target_pairs={{0,8},{8,0},{16,24},{24,16},{1,9},{9,1},{17,25},{25,17},{2,10},{10... | collective-permute-start | bytes 393224 | tf_op jit(solution)/shard_map/ppermute | solution.py:39
  53.6 1.9 %collective-permute-start.33 = (bf16[512,128]{1,0:T(8,128)(2,1)S(1)}, bf16[512,128]{1,0:T(8,128)(2,1)S(1)}, u32[]{:S(2)}, u32[]{:S(2)}) collective-permute-start(bf16[512,128]{1,0:T(8,128)(2,1)S(1)} %get-tuple-element.69), channel_id=1, source_target_pairs={{0,24},{8,16},{16,8},{24,0},{1,25},{9,17},{17,9},{25,1},{2,26},{10... | collective-permute-start | bytes 393224 | tf_op jit(solution)/shard_map/ppermute | solution.py:39
  55.6 2.5 %collective-permute-start.28 = (bf16[512,128]{1,0:T(8,128)(2,1)S(1)}, bf16[512,128]{1,0:T(8,128)(2,1)S(1)}, u32[]{:S(2)}, u32[]{:S(2)}) collective-permute-start(bf16[512,128]{1,0:T(8,128)(2,1)S(1)} %get-tuple-element.64), channel_id=1, source_target_pairs={{0,6},{1,7},{2,4},{3,5},{4,2},{5,3},{6,0},{7,1},{8,14},{9,15},{10,... | collective-permute-start | bytes 393224 | tf_op jit(solution)/shard_map/ppermute | solution.py:39
  58.6 1.6 %collective-permute-start.30 = (bf16[512,128]{1,0:T(8,128)(2,1)S(1)}, bf16[512,128]{1,0:T(8,128)(2,1)S(1)}, u32[]{:S(2)}, u32[]{:S(2)}) collective-permute-start(bf16[512,128]{1,0:T(8,128)(2,1)S(1)} %get-tuple-element.66), channel_id=1, source_target_pairs={{0,2},{1,3},{2,0},{3,1},{4,6},{5,7},{6,4},{7,5},{8,10},{9,11},{10,... | collective-permute-start | bytes 393224 | tf_op jit(solution)/shard_map/ppermute | solution.py:39
  60.2 5.8 %collective-permute-done.32.refs_9_ = bf16[512,128]{1,0:T(8,128)(2,1)S(1)} collective-permute-done((bf16[512,128]{1,0:T(8,128)(2,1)S(1)}, bf16[512,128]{1,0:T(8,128)(2,1)S(1)}, u32[]{:S(2)}, u32[]{:S(2)}) %collective-permute-start.32) | collective-permute-done | bytes 131104 | tf_op jit(solution)/shard_map/ppermute | solution.py:39
  66.2 2.5 %collective-permute-start.42 = (bf16[8,64,128]{2,1,0:T(8,128)(2,1)S(1)}, bf16[8,64,128]{2,1,0:T(8,128)(2,1)S(1)}, u32[]{:S(2)}, u32[]{:S(2)}) collective-permute-start(bf16[8,64,128]{2,1,0:T(8,128)(2,1)S(1)} %get-tuple-element.71.refs_2_.refs_3_), channel_id=1, source_target_pairs={{0,16},{8,24},{16,0},{24,8},{1,17},{9,25},{17,1},{25,9},{2,18},{10... | collective-permute-start | bytes 393224 | tf_op jit(solution)/shard_map/ppermute | solution.py:39
  68.9 1.7 %collective-permute-start.34 = (bf16[8,64,128]{2,1,0:T(8,128)(2,1)S(1)}, bf16[8,64,128]{2,1,0:T(8,128)(2,1)S(1)}, u32[]{:S(2)}, u32[]{:S(2)}) collective-permute-start(bf16[8,64,128]{2,1,0:T(8,128)(2,1)S(1)} %get-tuple-element.71.refs_2_.refs_3_), channel_id=1, source_target_pairs={{0,6},{1,7},{2,4},{3,5},{4,2},{5,3},{6,0},{7,1},{8,14},{9,15},{10,... | collective-permute-start | bytes 393224 | tf_op jit(solution)/shard_map/ppermute | solution.py:39
  70.6 1.2 %collective-permute-start.35 = (bf16[8,64,128]{2,1,0:T(8,128)(2,1)S(1)}, bf16[8,64,128]{2,1,0:T(8,128)(2,1)S(1)}, u32[]{:S(2)}, u32[]{:S(2)}) collective-permute-start(bf16[8,64,128]{2,1,0:T(8,128)(2,1)S(1)} %get-tuple-element.71.refs_2_.refs_3_), channel_id=1, source_target_pairs={{0,4},{1,5},{2,6},{3,7},{4,0},{5,1},{6,2},{7,3},{8,12},{9,13},{10,... | collective-permute-start | bytes 393224 | tf_op jit(solution)/shard_map/ppermute | solution.py:39
  71.8 0.7 collective-permute-start.36
  73.1 1.5 %collective-permute-done.41.refs_5_ = bf16[7,64,128]{2,1,0:T(8,128)(2,1)S(1)} collective-permute-done((bf16[7,64,128]{2,1,0:T(8,128)(2,1)S(1)}, bf16[7,64,128]{2,1,0:T(8,128)(2,1)S(1)}, u32[]{:S(2)}, u32[]{:S(2)}) %collective-permute-start.41) | collective-permute-done | bytes 114720 | tf_op jit(solution)/shard_map/ppermute | solution.py:39
  74.9 1.0 collective-permute-start.43
  77.4 0.8 collective-permute-done.39.refs_8_
  78.4 1.0 %shard_map.71.refs_1_ = bf16[64,4096]{1,0:T(8,128)(2,1)S(1)} custom-call(s32[3,32]{1,0:T(4,128)S(1)} %shard_map.59.refs_0_.refs_1_, bf16[32,128,128]{2,1,0:T(8,128)(2,1)S(1)} %bitcast.9, bf16[8,64,128]{2,1,0:T(8,128)(2,1)S(1)} %get-tuple-element.71.refs_2_.refs_3_, bf16[8,64,128]{2,1,0:T(8,128)(2,1)S(1)} %collective-permute-done.34.refs_3_, ...), custom_call_target="tpu_custom_call" | custom-call | flops 67108864 | bytes 2097536 | tf_op jit(solution)/shard_map/pallas_call | solution.py:25
  80.1 1.2 %shard_map.73 = f32[40,128]{1,0:T(8,128)S(1)} custom-call(s32[3,32]{1,0:T(4,128)S(1)} %shard_map.59.refs_0_.refs_1_, bf16[64,4096]{1,0:T(8,128)(2,1)S(1)} %shard_map.71.refs_1_, f32[64,128]{1,0:T(8,128)S(1)} %shard_map.72.refs_2_, bf16[8,64,128]{2,1,0:T(8,128)(2,1)S(1)} %get-tuple-element.71.refs_2_.refs_3_, ...), custom_call_target="tpu_custom_call" | custom-call | flops 33554432 | bytes 1081728 | tf_op jit(solution)/shard_map/pallas_call | solution.py:25
  81.4 1.2 %collective-permute-done.44 = f32[40,128]{1,0:T(8,128)S(1)} collective-permute-done((f32[40,128]{1,0:T(8,128)S(1)}, f32[40,128]{1,0:T(8,128)S(1)}, u32[]{:S(2)}, u32[]{:S(2)}) %collective-permute-start.44) | collective-permute-done | bytes 20512 | tf_op jit(solution)/shard_map/ppermute | solution.py:39
  82.6 1.4 %collective-permute-start.45 = (f32[40,128]{1,0:T(8,128)S(1)}, f32[40,128]{1,0:T(8,128)S(1)}, u32[]{:S(2)}, u32[]{:S(2)}) collective-permute-start(f32[40,128]{1,0:T(8,128)S(1)} %add.12), channel_id=1, source_target_pairs={{0,6},{1,7},{2,4},{3,5},{4,2},{5,3},{6,0},{7,1},{8,14},{9,15},{10,... | collective-permute-start | bytes 61448 | tf_op jit(solution)/shard_map/ppermute | solution.py:39
  83.9 1.2 %collective-permute-start.46 = (f32[40,128]{1,0:T(8,128)S(1)}, f32[40,128]{1,0:T(8,128)S(1)}, u32[]{:S(2)}, u32[]{:S(2)}) collective-permute-start(f32[40,128]{1,0:T(8,128)S(1)} %add.12), channel_id=1, source_target_pairs={{0,4},{1,5},{2,6},{3,7},{4,0},{5,1},{6,2},{7,3},{8,12},{9,13},{10,... | collective-permute-start | bytes 61448 | tf_op jit(solution)/shard_map/ppermute | solution.py:39
  85.1 0.9 collective-permute-start.47
  86.0 1.2 %collective-permute-done.45 = f32[40,128]{1,0:T(8,128)S(1)} collective-permute-done((f32[40,128]{1,0:T(8,128)S(1)}, f32[40,128]{1,0:T(8,128)S(1)}, u32[]{:S(2)}, u32[]{:S(2)}) %collective-permute-start.45) | collective-permute-done | bytes 20512 | tf_op jit(solution)/shard_map/ppermute | solution.py:39
  87.7 1.2 %collective-permute-done.47 = f32[40,128]{1,0:T(8,128)S(1)} collective-permute-done((f32[40,128]{1,0:T(8,128)S(1)}, f32[40,128]{1,0:T(8,128)S(1)}, u32[]{:S(2)}, u32[]{:S(2)}) %collective-permute-start.47) | collective-permute-done | bytes 20512 | tf_op jit(solution)/shard_map/ppermute | solution.py:39
  88.9 1.9 %collective-permute-start.48 = (f32[40,128]{1,0:T(8,128)S(1)}, f32[40,128]{1,0:T(8,128)S(1)}, u32[]{:S(2)}, u32[]{:S(2)}) collective-permute-start(f32[40,128]{1,0:T(8,128)S(1)} %add_add_fusion.refs_1_), channel_id=1, source_target_pairs={{0,24},{8,16},{16,8},{24,0},{1,25},{9,17},{17,9},{25,1},{2,26},{10... | collective-permute-start | bytes 61448 | tf_op jit(solution)/shard_map/ppermute | solution.py:39
  90.8 0.9 collective-permute-start.49
  91.7 1.7 %collective-permute-start.50 = (f32[40,128]{1,0:T(8,128)S(1)}, f32[40,128]{1,0:T(8,128)S(1)}, u32[]{:S(2)}, u32[]{:S(2)}) collective-permute-start(f32[40,128]{1,0:T(8,128)S(1)} %add_add_fusion.refs_1_), channel_id=1, source_target_pairs={{0,8},{8,0},{16,24},{24,16},{1,9},{9,1},{17,25},{25,17},{2,10},{10... | collective-permute-start | bytes 61448 | tf_op jit(solution)/shard_map/ppermute | solution.py:39
  93.4 1.2 %collective-permute-done.48.refs_2_ = f32[40,128]{1,0:T(8,128)S(1)} collective-permute-done((f32[40,128]{1,0:T(8,128)S(1)}, f32[40,128]{1,0:T(8,128)S(1)}, u32[]{:S(2)}, u32[]{:S(2)}) %collective-permute-start.48) | collective-permute-done | bytes 20512 | tf_op jit(solution)/shard_map/ppermute | solution.py:39
  94.6 1.2 %collective-permute-done.49.refs_3_ = f32[40,128]{1,0:T(8,128)S(1)} collective-permute-done((f32[40,128]{1,0:T(8,128)S(1)}, f32[40,128]{1,0:T(8,128)S(1)}, u32[]{:S(2)}, u32[]{:S(2)}) %collective-permute-start.49) | collective-permute-done | bytes 20512 | tf_op jit(solution)/shard_map/ppermute | solution.py:39
  95.7 3.8 %shard_map.74 = (f32[64,1024]{1,0:T(8,128)}, f32[64,64]{1,0:T(8,128)}) custom-call(f32[64,1024]{1,0:T(8,128)S(1)} %get-tuple-element.70.refs_0_, f32[40,128]{1,0:T(8,128)S(1)} %add_add_fusion.refs_1_, f32[40,128]{1,0:T(8,128)S(1)} %collective-permute-done.48.refs_2_, f32[40,128]{1,0:T(8,128)S(1)} %collective-permute-done.49.refs_3_, ...), custom_call_target="tpu_custom_call" | custom-call | bytes 344064 | tf_op jit(solution)/shard_map/pallas_call | solution.py:25
  (94 shorter events, 15.4 us)
Async XLA Ops:
  1.6 11.5 %collective-permute-start.8 = (bf16[8,64,128]{2,1,0:T(8,128)(2,1)S(1)}, bf16[8,64,128]{2,1,0:T(8,128)(2,1)S(1)}, u32[]{:S(2)}, u32[]{:S(2)}) collective-permute-start(bf16[8,64,128]{2,1,0:T(8,128)(2,1)S(1)} %shard_map.60.refs_2_.refs_3_), channel_id=1, source_target_pairs={{0,16},{8,24},{16,0},{24,8},{1,17},{9,25},{17,1},{25,9},{2,18},{10... | collective-permute-start | bytes 393224 | tf_op jit(solution)/shard_map/ppermute | solution.py:39
  5.7 7.3 %collective-permute-start.7 = (bf16[7,64,128]{2,1,0:T(8,128)(2,1)S(1)}, bf16[7,64,128]{2,1,0:T(8,128)(2,1)S(1)}, u32[]{:S(2)}, u32[]{:S(2)}) collective-permute-start(bf16[7,64,128]{2,1,0:T(8,128)(2,1)S(1)} %slice.24), channel_id=1, source_target_pairs={{0,8},{8,0},{16,24},{24,16},{1,9},{9,1},{17,25},{25,17},{2,10},{10... | collective-permute-start | bytes 344072 | tf_op jit(solution)/shard_map/ppermute | solution.py:39
  7.4 6.6 %collective-permute-start = (bf16[8,64,128]{2,1,0:T(8,128)(2,1)S(1)}, bf16[8,64,128]{2,1,0:T(8,128)(2,1)S(1)}, u32[]{:S(2)}, u32[]{:S(2)}) collective-permute-start(bf16[8,64,128]{2,1,0:T(8,128)(2,1)S(1)} %shard_map.60.refs_2_.refs_3_), channel_id=1, source_target_pairs={{0,6},{1,7},{2,4},{3,5},{4,2},{5,3},{6,0},{7,1},{8,14},{9,15},{10,... | collective-permute-start | bytes 393224 | tf_op jit(solution)/shard_map/ppermute | solution.py:39
  9.8 5.9 %collective-permute-start.1 = (bf16[8,64,128]{2,1,0:T(8,128)(2,1)S(1)}, bf16[8,64,128]{2,1,0:T(8,128)(2,1)S(1)}, u32[]{:S(2)}, u32[]{:S(2)}) collective-permute-start(bf16[8,64,128]{2,1,0:T(8,128)(2,1)S(1)} %shard_map.60.refs_2_.refs_3_), channel_id=1, source_target_pairs={{0,4},{1,5},{2,6},{3,7},{4,0},{5,1},{6,2},{7,3},{8,12},{9,13},{10,... | collective-permute-start | bytes 393224 | tf_op jit(solution)/shard_map/ppermute | solution.py:39
  10.3 5.5 %collective-permute-start.2 = (bf16[8,64,128]{2,1,0:T(8,128)(2,1)S(1)}, bf16[8,64,128]{2,1,0:T(8,128)(2,1)S(1)}, u32[]{:S(2)}, u32[]{:S(2)}) collective-permute-start(bf16[8,64,128]{2,1,0:T(8,128)(2,1)S(1)} %shard_map.60.refs_2_.refs_3_), channel_id=1, source_target_pairs={{0,2},{1,3},{2,0},{3,1},{4,6},{5,7},{6,4},{7,5},{8,10},{9,11},{10,... | collective-permute-start | bytes 393224 | tf_op jit(solution)/shard_map/ppermute | solution.py:39
  13.1 6.6 %collective-permute-start.9 = (bf16[9,64,128]{2,1,0:T(8,128)(2,1)S(1)}, bf16[9,64,128]{2,1,0:T(8,128)(2,1)S(1)}, u32[]{:S(2)}, u32[]{:S(2)}) collective-permute-start(bf16[9,64,128]{2,1,0:T(8,128)(2,1)S(1)} %pad_maximum_fusion), channel_id=1, source_target_pairs={{0,8},{8,0},{16,24},{24,16},{1,9},{9,1},{17,25},{25,17},{2,10},{10... | collective-permute-start | bytes 442376 | tf_op jit(solution)/shard_map/ppermute | solution.py:39
  13.6 2.6 %collective-permute-start.3 = (bf16[8,64,128]{2,1,0:T(8,128)(2,1)S(1)}, bf16[8,64,128]{2,1,0:T(8,128)(2,1)S(1)}, u32[]{:S(2)}, u32[]{:S(2)}) collective-permute-start(bf16[8,64,128]{2,1,0:T(8,128)(2,1)S(1)} %shard_map.60.refs_2_.refs_3_), channel_id=1, source_target_pairs={{0,1},{1,0},{2,3},{3,2},{4,5},{5,4},{6,7},{7,6},{8,9},{9,8},{10,11... | collective-permute-start | bytes 393224 | tf_op jit(solution)/shard_map/ppermute | solution.py:39
  13.9 2.3 %collective-permute-start.4 = (bf16[8,64,128]{2,1,0:T(8,128)(2,1)S(1)}, bf16[8,64,128]{2,1,0:T(8,128)(2,1)S(1)}, u32[]{:S(2)}, u32[]{:S(2)}) collective-permute-start(bf16[8,64,128]{2,1,0:T(8,128)(2,1)S(1)} %collective-permute-done.refs_3_), channel_id=1, source_target_pairs={{0,1},{1,0},{2,3},{3,2},{4,5},{5,4},{6,7},{7,6},{8,9},{9,8},{10,11... | collective-permute-start | bytes 393224 | tf_op jit(solution)/shard_map/ppermute | solution.py:39
  15.7 1.3 %collective-permute-start.5 = (bf16[8,64,128]{2,1,0:T(8,128)(2,1)S(1)}, bf16[8,64,128]{2,1,0:T(8,128)(2,1)S(1)}, u32[]{:S(2)}, u32[]{:S(2)}) collective-permute-start(bf16[8,64,128]{2,1,0:T(8,128)(2,1)S(1)} %collective-permute-done.1.refs_4_), channel_id=1, source_target_pairs={{0,1},{1,0},{2,3},{3,2},{4,5},{5,4},{6,7},{7,6},{8,9},{9,8},{10,11... | collective-permute-start | bytes 393224 | tf_op jit(solution)/shard_map/ppermute | solution.py:39
  15.8 1.4 %collective-permute-start.6 = (bf16[8,64,128]{2,1,0:T(8,128)(2,1)S(1)}, bf16[8,64,128]{2,1,0:T(8,128)(2,1)S(1)}, u32[]{:S(2)}, u32[]{:S(2)}) collective-permute-start(bf16[8,64,128]{2,1,0:T(8,128)(2,1)S(1)} %collective-permute-done.2.refs_5_), channel_id=1, source_target_pairs={{0,1},{1,0},{2,3},{3,2},{4,5},{5,4},{6,7},{7,6},{8,9},{9,8},{10,11... | collective-permute-start | bytes 393224 | tf_op jit(solution)/shard_map/ppermute | solution.py:39
  21.3 4.8 %collective-permute-start.10 = (bf16[4,528,128]{2,1,0:T(8,128)(2,1)S(1)}, bf16[4,528,128]{2,1,0:T(8,128)(2,1)S(1)}, u32[]{:S(2)}, u32[]{:S(2)}) collective-permute-start(bf16[4,528,128]{2,1,0:T(8,128)(2,1)S(1)} %get-tuple-element.44), channel_id=1, source_target_pairs={{0,1},{1,0},{2,3},{3,2},{4,5},{5,4},{6,7},{7,6},{8,9},{9,8},{10,11... | collective-permute-start | bytes 1622024 | tf_op jit(solution)/shard_map/ppermute | solution.py:39
  21.7 7.8 %collective-permute-start.14 = (bf16[528,128]{1,0:T(8,128)(2,1)S(1)}, bf16[528,128]{1,0:T(8,128)(2,1)S(1)}, u32[]{:S(2)}, u32[]{:S(2)}) collective-permute-start(bf16[528,128]{1,0:T(8,128)(2,1)S(1)} %get-tuple-element.50), channel_id=1, source_target_pairs={{0,8},{8,0},{16,24},{24,16},{1,9},{9,1},{17,25},{25,17},{2,10},{10... | collective-permute-start | bytes 405512 | tf_op jit(solution)/shard_map/ppermute | solution.py:39
  22.1 13.2 %collective-permute-start.15 = (bf16[528,128]{1,0:T(8,128)(2,1)S(1)}, bf16[528,128]{1,0:T(8,128)(2,1)S(1)}, u32[]{:S(2)}, u32[]{:S(2)}) collective-permute-start(bf16[528,128]{1,0:T(8,128)(2,1)S(1)} %get-tuple-element.51), channel_id=1, source_target_pairs={{0,16},{8,24},{16,0},{24,8},{1,17},{9,25},{17,1},{25,9},{2,18},{10... | collective-permute-start | bytes 405512 | tf_op jit(solution)/shard_map/ppermute | solution.py:39
  23.6 11.7 %collective-permute-start.16 = (bf16[528,128]{1,0:T(8,128)(2,1)S(1)}, bf16[528,128]{1,0:T(8,128)(2,1)S(1)}, u32[]{:S(2)}, u32[]{:S(2)}) collective-permute-start(bf16[528,128]{1,0:T(8,128)(2,1)S(1)} %get-tuple-element.52), channel_id=1, source_target_pairs={{0,24},{8,16},{16,8},{24,0},{1,25},{9,17},{17,9},{25,1},{2,26},{10... | collective-permute-start | bytes 405512 | tf_op jit(solution)/shard_map/ppermute | solution.py:39
  26.2 9.1 %collective-permute-start.11 = (bf16[528,128]{1,0:T(8,128)(2,1)S(1)}, bf16[528,128]{1,0:T(8,128)(2,1)S(1)}, u32[]{:S(2)}, u32[]{:S(2)}) collective-permute-start(bf16[528,128]{1,0:T(8,128)(2,1)S(1)} %get-tuple-element.47), channel_id=1, source_target_pairs={{0,6},{1,7},{2,4},{3,5},{4,2},{5,3},{6,0},{7,1},{8,14},{9,15},{10,... | collective-permute-start | bytes 405512 | tf_op jit(solution)/shard_map/ppermute | solution.py:39
  28.0 7.3 %collective-permute-start.12 = (bf16[528,128]{1,0:T(8,128)(2,1)S(1)}, bf16[528,128]{1,0:T(8,128)(2,1)S(1)}, u32[]{:S(2)}, u32[]{:S(2)}) collective-permute-start(bf16[528,128]{1,0:T(8,128)(2,1)S(1)} %get-tuple-element.48), channel_id=1, source_target_pairs={{0,4},{1,5},{2,6},{3,7},{4,0},{5,1},{6,2},{7,3},{8,12},{9,13},{10,... | collective-permute-start | bytes 405512 | tf_op jit(solution)/shard_map/ppermute | solution.py:39
  29.4 5.9 %collective-permute-start.13 = (bf16[528,128]{1,0:T(8,128)(2,1)S(1)}, bf16[528,128]{1,0:T(8,128)(2,1)S(1)}, u32[]{:S(2)}, u32[]{:S(2)}) collective-permute-start(bf16[528,128]{1,0:T(8,128)(2,1)S(1)} %get-tuple-element.49), channel_id=1, source_target_pairs={{0,2},{1,3},{2,0},{3,1},{4,6},{5,7},{6,4},{7,5},{8,10},{9,11},{10,... | collective-permute-start | bytes 405512 | tf_op jit(solution)/shard_map/ppermute | solution.py:39
  35.5 8.7 %collective-permute-start.25 = (bf16[8,64,128]{2,1,0:T(8,128)(2,1)S(1)}, bf16[8,64,128]{2,1,0:T(8,128)(2,1)S(1)}, u32[]{:S(2)}, u32[]{:S(2)}) collective-permute-start(bf16[8,64,128]{2,1,0:T(8,128)(2,1)S(1)} %get-tuple-element.55.refs_2_.refs_3_), channel_id=1, source_target_pairs={{0,16},{8,24},{16,0},{24,8},{1,17},{9,25},{17,1},{25,9},{2,18},{10... | collective-permute-start | bytes 393224 | tf_op jit(solution)/shard_map/ppermute | solution.py:39
  38.5 5.5 %collective-permute-start.24 = (bf16[7,64,128]{2,1,0:T(8,128)(2,1)S(1)}, bf16[7,64,128]{2,1,0:T(8,128)(2,1)S(1)}, u32[]{:S(2)}, u32[]{:S(2)}) collective-permute-start(bf16[7,64,128]{2,1,0:T(8,128)(2,1)S(1)} %slice.20), channel_id=1, source_target_pairs={{0,8},{8,0},{16,24},{24,16},{1,9},{9,1},{17,25},{25,17},{2,10},{10... | collective-permute-start | bytes 344072 | tf_op jit(solution)/shard_map/ppermute | solution.py:39
  38.6 7.0 %collective-permute-start.17 = (bf16[8,64,128]{2,1,0:T(8,128)(2,1)S(1)}, bf16[8,64,128]{2,1,0:T(8,128)(2,1)S(1)}, u32[]{:S(2)}, u32[]{:S(2)}) collective-permute-start(bf16[8,64,128]{2,1,0:T(8,128)(2,1)S(1)} %get-tuple-element.55.refs_2_.refs_3_), channel_id=1, source_target_pairs={{0,6},{1,7},{2,4},{3,5},{4,2},{5,3},{6,0},{7,1},{8,14},{9,15},{10,... | collective-permute-start | bytes 393224 | tf_op jit(solution)/shard_map/ppermute | solution.py:39
  41.1 5.5 %collective-permute-start.18 = (bf16[8,64,128]{2,1,0:T(8,128)(2,1)S(1)}, bf16[8,64,128]{2,1,0:T(8,128)(2,1)S(1)}, u32[]{:S(2)}, u32[]{:S(2)}) collective-permute-start(bf16[8,64,128]{2,1,0:T(8,128)(2,1)S(1)} %get-tuple-element.55.refs_2_.refs_3_), channel_id=1, source_target_pairs={{0,4},{1,5},{2,6},{3,7},{4,0},{5,1},{6,2},{7,3},{8,12},{9,13},{10,... | collective-permute-start | bytes 393224 | tf_op jit(solution)/shard_map/ppermute | solution.py:39
  41.6 5.1 %collective-permute-start.19 = (bf16[8,64,128]{2,1,0:T(8,128)(2,1)S(1)}, bf16[8,64,128]{2,1,0:T(8,128)(2,1)S(1)}, u32[]{:S(2)}, u32[]{:S(2)}) collective-permute-start(bf16[8,64,128]{2,1,0:T(8,128)(2,1)S(1)} %get-tuple-element.55.refs_2_.refs_3_), channel_id=1, source_target_pairs={{0,2},{1,3},{2,0},{3,1},{4,6},{5,7},{6,4},{7,5},{8,10},{9,11},{10,... | collective-permute-start | bytes 393224 | tf_op jit(solution)/shard_map/ppermute | solution.py:39
  44.2 5.2 %collective-permute-start.26 = (bf16[9,64,128]{2,1,0:T(8,128)(2,1)S(1)}, bf16[9,64,128]{2,1,0:T(8,128)(2,1)S(1)}, u32[]{:S(2)}, u32[]{:S(2)}) collective-permute-start(bf16[9,64,128]{2,1,0:T(8,128)(2,1)S(1)} %pad_maximum_fusion.1), channel_id=1, source_target_pairs={{0,8},{8,0},{16,24},{24,16},{1,9},{9,1},{17,25},{25,17},{2,10},{10... | collective-permute-start | bytes 442376 | tf_op jit(solution)/shard_map/ppermute | solution.py:39
  45.6 1.6 %collective-permute-start.20 = (bf16[8,64,128]{2,1,0:T(8,128)(2,1)S(1)}, bf16[8,64,128]{2,1,0:T(8,128)(2,1)S(1)}, u32[]{:S(2)}, u32[]{:S(2)}) collective-permute-start(bf16[8,64,128]{2,1,0:T(8,128)(2,1)S(1)} %get-tuple-element.55.refs_2_.refs_3_), channel_id=1, source_target_pairs={{0,1},{1,0},{2,3},{3,2},{4,5},{5,4},{6,7},{7,6},{8,9},{9,8},{10,11... | collective-permute-start | bytes 393224 | tf_op jit(solution)/shard_map/ppermute | solution.py:39
  45.6 1.5 %collective-permute-start.21 = (bf16[8,64,128]{2,1,0:T(8,128)(2,1)S(1)}, bf16[8,64,128]{2,1,0:T(8,128)(2,1)S(1)}, u32[]{:S(2)}, u32[]{:S(2)}) collective-permute-start(bf16[8,64,128]{2,1,0:T(8,128)(2,1)S(1)} %collective-permute-done.17.refs_3_), channel_id=1, source_target_pairs={{0,1},{1,0},{2,3},{3,2},{4,5},{5,4},{6,7},{7,6},{8,9},{9,8},{10,11... | collective-permute-start | bytes 393224 | tf_op jit(solution)/shard_map/ppermute | solution.py:39
  46.6 1.3 %collective-permute-start.22 = (bf16[8,64,128]{2,1,0:T(8,128)(2,1)S(1)}, bf16[8,64,128]{2,1,0:T(8,128)(2,1)S(1)}, u32[]{:S(2)}, u32[]{:S(2)}) collective-permute-start(bf16[8,64,128]{2,1,0:T(8,128)(2,1)S(1)} %collective-permute-done.18.refs_4_), channel_id=1, source_target_pairs={{0,1},{1,0},{2,3},{3,2},{4,5},{5,4},{6,7},{7,6},{8,9},{9,8},{10,11... | collective-permute-start | bytes 393224 | tf_op jit(solution)/shard_map/ppermute | solution.py:39
  46.7 1.5 %collective-permute-start.23 = (bf16[8,64,128]{2,1,0:T(8,128)(2,1)S(1)}, bf16[8,64,128]{2,1,0:T(8,128)(2,1)S(1)}, u32[]{:S(2)}, u32[]{:S(2)}) collective-permute-start(bf16[8,64,128]{2,1,0:T(8,128)(2,1)S(1)} %collective-permute-done.19.refs_5_), channel_id=1, source_target_pairs={{0,1},{1,0},{2,3},{3,2},{4,5},{5,4},{6,7},{7,6},{8,9},{9,8},{10,11... | collective-permute-start | bytes 393224 | tf_op jit(solution)/shard_map/ppermute | solution.py:39
  50.9 4.6 %collective-permute-start.27 = (bf16[4,512,128]{2,1,0:T(8,128)(2,1)S(1)}, bf16[4,512,128]{2,1,0:T(8,128)(2,1)S(1)}, u32[]{:S(2)}, u32[]{:S(2)}) collective-permute-start(bf16[4,512,128]{2,1,0:T(8,128)(2,1)S(1)} %get-tuple-element.62), channel_id=1, source_target_pairs={{0,1},{1,0},{2,3},{3,2},{4,5},{5,4},{6,7},{7,6},{8,9},{9,8},{10,11... | collective-permute-start | bytes 1572872 | tf_op jit(solution)/shard_map/ppermute | solution.py:39
  51.1 7.5 %collective-permute-start.31 = (bf16[512,128]{1,0:T(8,128)(2,1)S(1)}, bf16[512,128]{1,0:T(8,128)(2,1)S(1)}, u32[]{:S(2)}, u32[]{:S(2)}) collective-permute-start(bf16[512,128]{1,0:T(8,128)(2,1)S(1)} %get-tuple-element.67), channel_id=1, source_target_pairs={{0,8},{8,0},{16,24},{24,16},{1,9},{9,1},{17,25},{25,17},{2,10},{10... | collective-permute-start | bytes 393224 | tf_op jit(solution)/shard_map/ppermute | solution.py:39
  53.1 12.9 %collective-permute-start.32 = (bf16[512,128]{1,0:T(8,128)(2,1)S(1)}, bf16[512,128]{1,0:T(8,128)(2,1)S(1)}, u32[]{:S(2)}, u32[]{:S(2)}) collective-permute-start(bf16[512,128]{1,0:T(8,128)(2,1)S(1)} %get-tuple-element.68), channel_id=1, source_target_pairs={{0,16},{8,24},{16,0},{24,8},{1,17},{9,25},{17,1},{25,9},{2,18},{10... | collective-permute-start | bytes 393224 | tf_op jit(solution)/shard_map/ppermute | solution.py:39
  53.6 12.4 %collective-permute-start.33 = (bf16[512,128]{1,0:T(8,128)(2,1)S(1)}, bf16[512,128]{1,0:T(8,128)(2,1)S(1)}, u32[]{:S(2)}, u32[]{:S(2)}) collective-permute-start(bf16[512,128]{1,0:T(8,128)(2,1)S(1)} %get-tuple-element.69), channel_id=1, source_target_pairs={{0,24},{8,16},{16,8},{24,0},{1,25},{9,17},{17,9},{25,1},{2,26},{10... | collective-permute-start | bytes 393224 | tf_op jit(solution)/shard_map/ppermute | solution.py:39
  55.6 10.4 %collective-permute-start.28 = (bf16[512,128]{1,0:T(8,128)(2,1)S(1)}, bf16[512,128]{1,0:T(8,128)(2,1)S(1)}, u32[]{:S(2)}, u32[]{:S(2)}) collective-permute-start(bf16[512,128]{1,0:T(8,128)(2,1)S(1)} %get-tuple-element.64), channel_id=1, source_target_pairs={{0,6},{1,7},{2,4},{3,5},{4,2},{5,3},{6,0},{7,1},{8,14},{9,15},{10,... | collective-permute-start | bytes 393224 | tf_op jit(solution)/shard_map/ppermute | solution.py:39
  58.1 8.0 %collective-permute-start.29 = (bf16[512,128]{1,0:T(8,128)(2,1)S(1)}, bf16[512,128]{1,0:T(8,128)(2,1)S(1)}, u32[]{:S(2)}, u32[]{:S(2)}) collective-permute-start(bf16[512,128]{1,0:T(8,128)(2,1)S(1)} %get-tuple-element.65), channel_id=1, source_target_pairs={{0,4},{1,5},{2,6},{3,7},{4,0},{5,1},{6,2},{7,3},{8,12},{9,13},{10,... | collective-permute-start | bytes 393224 | tf_op jit(solution)/shard_map/ppermute | solution.py:39
  58.6 7.4 %collective-permute-start.30 = (bf16[512,128]{1,0:T(8,128)(2,1)S(1)}, bf16[512,128]{1,0:T(8,128)(2,1)S(1)}, u32[]{:S(2)}, u32[]{:S(2)}) collective-permute-start(bf16[512,128]{1,0:T(8,128)(2,1)S(1)} %get-tuple-element.66), channel_id=1, source_target_pairs={{0,2},{1,3},{2,0},{3,1},{4,6},{5,7},{6,4},{7,5},{8,10},{9,11},{10,... | collective-permute-start | bytes 393224 | tf_op jit(solution)/shard_map/ppermute | solution.py:39
  66.2 8.6 %collective-permute-start.42 = (bf16[8,64,128]{2,1,0:T(8,128)(2,1)S(1)}, bf16[8,64,128]{2,1,0:T(8,128)(2,1)S(1)}, u32[]{:S(2)}, u32[]{:S(2)}) collective-permute-start(bf16[8,64,128]{2,1,0:T(8,128)(2,1)S(1)} %get-tuple-element.71.refs_2_.refs_3_), channel_id=1, source_target_pairs={{0,16},{8,24},{16,0},{24,8},{1,17},{9,25},{17,1},{25,9},{2,18},{10... | collective-permute-start | bytes 393224 | tf_op jit(solution)/shard_map/ppermute | solution.py:39
  68.8 5.8 %collective-permute-start.41 = (bf16[7,64,128]{2,1,0:T(8,128)(2,1)S(1)}, bf16[7,64,128]{2,1,0:T(8,128)(2,1)S(1)}, u32[]{:S(2)}, u32[]{:S(2)}) collective-permute-start(bf16[7,64,128]{2,1,0:T(8,128)(2,1)S(1)} %slice.22), channel_id=1, source_target_pairs={{0,8},{8,0},{16,24},{24,16},{1,9},{9,1},{17,25},{25,17},{2,10},{10... | collective-permute-start | bytes 344072 | tf_op jit(solution)/shard_map/ppermute | solution.py:39
  68.9 7.2 %collective-permute-start.34 = (bf16[8,64,128]{2,1,0:T(8,128)(2,1)S(1)}, bf16[8,64,128]{2,1,0:T(8,128)(2,1)S(1)}, u32[]{:S(2)}, u32[]{:S(2)}) collective-permute-start(bf16[8,64,128]{2,1,0:T(8,128)(2,1)S(1)} %get-tuple-element.71.refs_2_.refs_3_), channel_id=1, source_target_pairs={{0,6},{1,7},{2,4},{3,5},{4,2},{5,3},{6,0},{7,1},{8,14},{9,15},{10,... | collective-permute-start | bytes 393224 | tf_op jit(solution)/shard_map/ppermute | solution.py:39
  70.6 6.2 %collective-permute-start.35 = (bf16[8,64,128]{2,1,0:T(8,128)(2,1)S(1)}, bf16[8,64,128]{2,1,0:T(8,128)(2,1)S(1)}, u32[]{:S(2)}, u32[]{:S(2)}) collective-permute-start(bf16[8,64,128]{2,1,0:T(8,128)(2,1)S(1)} %get-tuple-element.71.refs_2_.refs_3_), channel_id=1, source_target_pairs={{0,4},{1,5},{2,6},{3,7},{4,0},{5,1},{6,2},{7,3},{8,12},{9,13},{10,... | collective-permute-start | bytes 393224 | tf_op jit(solution)/shard_map/ppermute | solution.py:39
  71.8 5.1 %collective-permute-start.36 = (bf16[8,64,128]{2,1,0:T(8,128)(2,1)S(1)}, bf16[8,64,128]{2,1,0:T(8,128)(2,1)S(1)}, u32[]{:S(2)}, u32[]{:S(2)}) collective-permute-start(bf16[8,64,128]{2,1,0:T(8,128)(2,1)S(1)} %get-tuple-element.71.refs_2_.refs_3_), channel_id=1, source_target_pairs={{0,2},{1,3},{2,0},{3,1},{4,6},{5,7},{6,4},{7,5},{8,10},{9,11},{10,... | collective-permute-start | bytes 393224 | tf_op jit(solution)/shard_map/ppermute | solution.py:39
  74.9 5.2 %collective-permute-start.43 = (bf16[9,64,128]{2,1,0:T(8,128)(2,1)S(1)}, bf16[9,64,128]{2,1,0:T(8,128)(2,1)S(1)}, u32[]{:S(2)}, u32[]{:S(2)}) collective-permute-start(bf16[9,64,128]{2,1,0:T(8,128)(2,1)S(1)} %pad_maximum_fusion.2), channel_id=1, source_target_pairs={{0,8},{8,0},{16,24},{24,16},{1,9},{9,1},{17,25},{25,17},{2,10},{10... | collective-permute-start | bytes 442376 | tf_op jit(solution)/shard_map/ppermute | solution.py:39
  75.9 1.5 %collective-permute-start.37 = (bf16[8,64,128]{2,1,0:T(8,128)(2,1)S(1)}, bf16[8,64,128]{2,1,0:T(8,128)(2,1)S(1)}, u32[]{:S(2)}, u32[]{:S(2)}) collective-permute-start(bf16[8,64,128]{2,1,0:T(8,128)(2,1)S(1)} %get-tuple-element.71.refs_2_.refs_3_), channel_id=1, source_target_pairs={{0,1},{1,0},{2,3},{3,2},{4,5},{5,4},{6,7},{7,6},{8,9},{9,8},{10,11... | collective-permute-start | bytes 393224 | tf_op jit(solution)/shard_map/ppermute | solution.py:39
  76.9 1.5 %collective-permute-start.40 = (bf16[8,64,128]{2,1,0:T(8,128)(2,1)S(1)}, bf16[8,64,128]{2,1,0:T(8,128)(2,1)S(1)}, u32[]{:S(2)}, u32[]{:S(2)}) collective-permute-start(bf16[8,64,128]{2,1,0:T(8,128)(2,1)S(1)} %collective-permute-done.36.refs_5_), channel_id=1, source_target_pairs={{0,1},{1,0},{2,3},{3,2},{4,5},{5,4},{6,7},{7,6},{8,9},{9,8},{10,11... | collective-permute-start | bytes 393224 | tf_op jit(solution)/shard_map/ppermute | solution.py:39
  82.6 4.7 %collective-permute-start.45 = (f32[40,128]{1,0:T(8,128)S(1)}, f32[40,128]{1,0:T(8,128)S(1)}, u32[]{:S(2)}, u32[]{:S(2)}) collective-permute-start(f32[40,128]{1,0:T(8,128)S(1)} %add.12), channel_id=1, source_target_pairs={{0,6},{1,7},{2,4},{3,5},{4,2},{5,3},{6,0},{7,1},{8,14},{9,15},{10,... | collective-permute-start | bytes 61448 | tf_op jit(solution)/shard_map/ppermute | solution.py:39
  83.9 3.8 %collective-permute-start.46 = (f32[40,128]{1,0:T(8,128)S(1)}, f32[40,128]{1,0:T(8,128)S(1)}, u32[]{:S(2)}, u32[]{:S(2)}) collective-permute-start(f32[40,128]{1,0:T(8,128)S(1)} %add.12), channel_id=1, source_target_pairs={{0,4},{1,5},{2,6},{3,7},{4,0},{5,1},{6,2},{7,3},{8,12},{9,13},{10,... | collective-permute-start | bytes 61448 | tf_op jit(solution)/shard_map/ppermute | solution.py:39
  85.1 3.8 %collective-permute-start.47 = (f32[40,128]{1,0:T(8,128)S(1)}, f32[40,128]{1,0:T(8,128)S(1)}, u32[]{:S(2)}, u32[]{:S(2)}) collective-permute-start(f32[40,128]{1,0:T(8,128)S(1)} %add.12), channel_id=1, source_target_pairs={{0,2},{1,3},{2,0},{3,1},{4,6},{5,7},{6,4},{7,5},{8,10},{9,11},{10,... | collective-permute-start | bytes 61448 | tf_op jit(solution)/shard_map/ppermute | solution.py:39
  88.9 5.6 %collective-permute-start.48 = (f32[40,128]{1,0:T(8,128)S(1)}, f32[40,128]{1,0:T(8,128)S(1)}, u32[]{:S(2)}, u32[]{:S(2)}) collective-permute-start(f32[40,128]{1,0:T(8,128)S(1)} %add_add_fusion.refs_1_), channel_id=1, source_target_pairs={{0,24},{8,16},{16,8},{24,0},{1,25},{9,17},{17,9},{25,1},{2,26},{10... | collective-permute-start | bytes 61448 | tf_op jit(solution)/shard_map/ppermute | solution.py:39
  90.8 4.9 %collective-permute-start.49 = (f32[40,128]{1,0:T(8,128)S(1)}, f32[40,128]{1,0:T(8,128)S(1)}, u32[]{:S(2)}, u32[]{:S(2)}) collective-permute-start(f32[40,128]{1,0:T(8,128)S(1)} %add_add_fusion.refs_1_), channel_id=1, source_target_pairs={{0,16},{8,24},{16,0},{24,8},{1,17},{9,25},{17,1},{25,9},{2,18},{10... | collective-permute-start | bytes 61448 | tf_op jit(solution)/shard_map/ppermute | solution.py:39
  91.7 4.0 %collective-permute-start.50 = (f32[40,128]{1,0:T(8,128)S(1)}, f32[40,128]{1,0:T(8,128)S(1)}, u32[]{:S(2)}, u32[]{:S(2)}) collective-permute-start(f32[40,128]{1,0:T(8,128)S(1)} %add_add_fusion.refs_1_), channel_id=1, source_target_pairs={{0,8},{8,0},{16,24},{24,16},{1,9},{9,1},{17,25},{25,17},{2,10},{10... | collective-permute-start | bytes 61448 | tf_op jit(solution)/shard_map/ppermute | solution.py:39
  (9 other events, 22.7 us)

commit v18 on v17

--- a/solution.py
+++ b/solution.py
@@ -17,6 +17,7 @@
 VMEM = pl.BlockSpec(memory_space=pltpu.VMEM)
 SMEM = pl.BlockSpec(memory_space=pltpu.SMEM)
 ANY = pl.BlockSpec(memory_space=pl.ANY)
+HBM = pl.BlockSpec(memory_space=pltpu.HBM)
 DEGREE_ROWS = 16
 
 
@@ -48,7 +49,19 @@
     return [ref[:, k * width : (k + 1) * width] for k in range(ref.shape[1] // width)]
 
 
-def round_kernel(vec_ref, out_ref):
+def bring(sources, targets, arrived):
+    copies = [
+        pltpu.make_async_copy(source, target, arrived.at[i])
+        for i, (source, target) in enumerate(zip(sources, targets))
+    ]
+    for copy in copies:
+        copy.start()
+    for copy in copies:
+        copy.wait()
+
+
+def round_kernel(source, out_ref, vec_ref, arrived):
+    bring([source], [vec_ref], arrived)
     for k, piece in enumerate(tiles_first(vec_ref, out_ref.shape[2])):
         out_ref[k] = piece.astype(BF16)
 
@@ -71,7 +84,8 @@
             at += count
 
 
-def table_kernel(group, meta, rows_ref, cols_ref, table):
+def table_kernel(group, rows_source, cols_source, meta, table, rows_ref, cols_ref, arrived):
+    bring([rows_source, cols_source], [rows_ref, cols_ref], arrived)
     rows, cols = rows_ref[...], cols_ref[...]
     apart = lax.div(rows, group) ^ meta[1]
     halves = lax.rem(apart, 2) * meta[2] + lax.div(apart, 2)
@@ -388,17 +402,17 @@
     row_runs = [[((2 * d + core) * group, group)] for core in range(2) for d in chip_order]
     runs = (col_runs, row_runs)
     def gather(rounded, first=()):
-        held = [rounded]
+        held, other = [rounded], trade(rounded, "col", 1)
         for d in levels:
             if len(held) == 1:
                 held += [trade(rounded, "row", d)]
                 continue
             near = trade(rounded[: group - late], "row", d)
-            near, *passed = lax.optimization_barrier((near, *held[1:], *first))
+            near, other, *passed = lax.optimization_barrier((near, other, *held[1:], *first))
             held[1:] = passed[: len(held) - 1]
             held += [near, trade(jnp.concatenate([rounded[group - late :], *held[1:]]), "row", d)]
         chips = [rounded, *exchange([rounded] * (chips_n - 1), "col", 2)[::-1]]
-        return held, chips + [trade(chip, "col", 1) for chip in chips]
+        return held, [*chips, other, *(trade(chip, "col", 1) for chip in chips[1:])]
 
     def apply(rounded, table, degree, first=()):
         height = vectors_n + (DEGREE_ROWS if degree else 0)
@@ -418,16 +432,22 @@
         row_got = exchange(row_send[len(row_degree) :], "col", 2)[::-1]
         return [*row_degree, row_own, col_own, *row_got, *col_got]
 
-    rounded = call(round_kernel, rounded_shape, [], 16, [start])
+    rounded = pl.pallas_call(
+        round_kernel,
+        out_shape=rounded_shape,
+        in_specs=[HBM],
+        out_specs=VMEM,
+        scratch_shapes=[pltpu.VMEM(start.shape, F32), pltpu.SemaphoreType.DMA((1,))],
+    )(start)
     meta = jnp.stack([lax.axis_index("row"), lax.axis_index("col"), chips_n]).astype(jnp.int32)
-    table = call(
+    indices = (1, tiles.shape[0])
+    table = pl.pallas_call(
         functools.partial(table_kernel, group),
-        jax.ShapeDtypeStruct((3, tiles.shape[0]), jnp.int32),
-        [],
-        16,
-        [meta, tile_rows[None], tile_cols[None]],
-        smem=1,
-    )
+        out_shape=jax.ShapeDtypeStruct((3, tiles.shape[0]), jnp.int32),
+        in_specs=[HBM, HBM, SMEM],
+        out_specs=VMEM,
+        scratch_shapes=[pltpu.VMEM(indices, jnp.int32)] * 2 + [pltpu.SemaphoreType.DMA((2,))],
+    )(tile_rows[None], tile_cols[None], meta)
     first, rounded, degree = call(
         functools.partial(first_kernel, chips_n),
         [vector_shape, rounded_shape, degree_shape],

time: 99.7 us -> 111 us (1.11)
  waiting for transfers between devices: 27.7 us -> 35.5 us
  Pallas kernels: 13.6 us -> 16.5 us
    ppermute x51, waiting for transfers between devices: 27.7 us -> 35.5 us  [trade(): return lax.ppermute(part, axis, [(i, i ^ d) for i in range(n)])]
    pallas_call x0 -> x2, Pallas kernels: none -> 3.57 us  [the longest x1 1.94 us: local(): pl.pallas_call(functools.partial(table_kernel, group), out_shape=jax.Shap...]
    pallas_call x16 -> x14, Pallas kernels: 13.6 us -> 13 us  [call(): pl.pallas_call(lambda *refs: kernel(*refs[len(after):]), out_shape=jax.tr...]
  transfers between devices with their start and end apart: 51 -> 51, of which waited for: 30 -> 24; matrix products, arithmetic and copies ran while one was open for 0% -> 1% of each run, Pallas kernels for 5% -> 6%
where the time goes in v18:
time: 111 us
  starting transfers between devices  52.8 us (48%)
  waiting for transfers between devices  35.5 us (32%)
  Pallas kernels  16.5 us (15%)
  local copies, waits for them, and re-layouts  4.47 us (4%)
    ppermute x51, starting transfers between devices, trade(): return lax.ppermute(part, axis, [(i, i ^ d) for i in range(n)])  52.8 us
    ppermute x51, waiting for transfers between devices, trade(): return lax.ppermute(part, axis, [(i, i ^ d) for i in range(n)])  35.5 us
    pallas_call x14, Pallas kernels, call(): pl.pallas_call(lambda *refs: kernel(*refs[len(after):]), out_shape=jax.tr...  13 us
    unnamed x12, local copies, waits for them, and re-layouts  2.82 us
  transfers between devices with their start and end apart: 51, of which 24 were waited for; matrix products, arithmetic and copies ran while one was open for 1% of the time, Pallas kernels for 6%

profile of v18, /device:TPU:0, one launch (start us, length us, event | category | flops | bytes accessed | tf_op | source)
XLA Modules:
  0.0 110.8 jit_solution(16219848979102662626)
XLA Ops:
  0.6 1.6 %shard_map.60.refs_2_.refs_3_ = bf16[8,64,128]{2,1,0:T(8,128)(2,1)} custom-call(f32[64,1024]{1,0:T(8,128)} %refs_0_.3), custom_call_target="tpu_custom_call" | custom-call | tf_op jit(solution)/shard_map/pallas_call | solution.py:435
  2.3 0.9 slice.24
  3.2 3.1 %collective-permute-start.3 = (bf16[7,64,128]{2,1,0:T(8,128)(2,1)S(1)}, bf16[7,64,128]{2,1,0:T(8,128)(2,1)S(1)}, u32[]{:S(2)}, u32[]{:S(2)}) collective-permute-start(bf16[7,64,128]{2,1,0:T(8,128)(2,1)S(1)} %slice.24), channel_id=1, source_target_pairs={{0,8},{8,0},{16,24},{24,16},{1,9},{9,1},{17,25},{25,17},{2,10},{10... | collective-permute-start | bytes 344072 | tf_op jit(solution)/shard_map/ppermute | solution.py:40
  6.3 2.6 %collective-permute-start.5 = (bf16[8,64,128]{2,1,0:T(8,128)(2,1)}, bf16[8,64,128]{2,1,0:T(8,128)(2,1)S(1)}, u32[]{:S(2)}, u32[]{:S(2)}) collective-permute-start(bf16[8,64,128]{2,1,0:T(8,128)(2,1)} %shard_map.60.refs_2_.refs_3_), channel_id=1, source_target_pairs={{0,16},{8,24},{16,0},{24,8},{1,17},{9,25},{17,1},{25,9},{2,18},{10... | collective-permute-start | bytes 393224 | tf_op jit(solution)/shard_map/ppermute | solution.py:40
  8.9 2.4 %collective-permute-start = (bf16[8,64,128]{2,1,0:T(8,128)(2,1)}, bf16[8,64,128]{2,1,0:T(8,128)(2,1)S(1)}, u32[]{:S(2)}, u32[]{:S(2)}) collective-permute-start(bf16[8,64,128]{2,1,0:T(8,128)(2,1)} %shard_map.60.refs_2_.refs_3_), channel_id=1, source_target_pairs={{0,6},{1,7},{2,4},{3,5},{4,2},{5,3},{6,0},{7,1},{8,14},{9,15},{10,... | collective-permute-start | bytes 393224 | tf_op jit(solution)/shard_map/ppermute | solution.py:40
  13.6 1.9 %shard_map.59.refs_0_.refs_1_ = s32[3,32]{1,0:T(4,128)} custom-call(s32[1,32]{1,0:T(1,128)} %bitcast.10, s32[1,32]{1,0:T(1,128)} %bitcast.11, s32[3]{0:T(128)} %pad_add_fusion.meta), custom_call_target="tpu_custom_call" | custom-call | tf_op jit(solution)/shard_map/pallas_call | solution.py:444
  16.4 2.0 %collective-permute-done.1.refs_4_ = bf16[8,64,128]{2,1,0:T(8,128)(2,1)S(1)} collective-permute-done((bf16[8,64,128]{2,1,0:T(8,128)(2,1)}, bf16[8,64,128]{2,1,0:T(8,128)(2,1)S(1)}, u32[]{:S(2)}, u32[]{:S(2)}) %collective-permute-start.1) | collective-permute-done | bytes 131104 | tf_op jit(solution)/shard_map/ppermute | solution.py:40
  19.9 1.2 %copy-done = bf16[1,1,32,128,128]{4,3,2,1,0:T(8,128)(2,1)S(1)} copy-done((bf16[1,1,32,128,128]{4,3,2,1,0:T(8,128)(2,1)S(1)}, bf16[1,1,32,128,128]{4,3,2,1,0:T(8,128)(2,1)}, u32[]{:S(2)}) %copy-start) | copy-done | bytes 1048600
  21.2 0.9 copy-done.3
  22.8 1.2 %shard_map.62 = (f32[8,80,128]{2,1,0:T(8,128)S(1)}, f32[32,80,128]{2,1,0:T(8,128)S(1)}, bf16[528,128]{1,0:T(8,128)(2,1)S(1)}, bf16[528,128]{1,0:T(8,128)(2,1)S(1)}, bf16[528,128]{1,0:T(8,128)(2,1)S(1)}) custom-call(s32[3,32]{1,0:T(4,128)S(1)} %copy-done.4, bf16[32,128,128]{2,1,0:T(8,128)(2,1)S(1)} %bitcast.5, ...), custom_call_target="tpu_custom_call", output_to_operand_aliasing={{1}: (10, {})} | custom-call | flops 67108864 | bytes 3408256 | tf_op jit(solution)/shard_map/pallas_call | solution.py:26
  24.0 1.5 %shard_map.63 = (f32[64,80,128]{2,1,0:T(8,128)S(1)}, bf16[4,528,128]{2,1,0:T(8,128)(2,1)S(1)}) custom-call(f32[8,80,128]{2,1,0:T(8,128)S(1)} %get-tuple-element.44.refs_0_.refs_3_, s32[3,32]{1,0:T(4,128)S(1)} %copy-done.4, bf16[32,128,128]{2,1,0:T(8,128)(2,1)S(1)} %bitcast.6, bf16[8,64,128]{2,1,0:T(8,128)(2,1)S(1)} %copy-done.3, ...), custom_call_target="tpu_custom_call", output_to_operand_aliasing={{0}: (7, {})} | custom-call | flops 67108864 | bytes 4194688 | tf_op jit(solution)/shard_map/pallas_call | solution.py:26
  26.4 1.8 %collective-permute-start.15 = (bf16[528,128]{1,0:T(8,128)(2,1)S(1)}, bf16[528,128]{1,0:T(8,128)(2,1)S(1)}, u32[]{:S(2)}, u32[]{:S(2)}) collective-permute-start(bf16[528,128]{1,0:T(8,128)(2,1)S(1)} %get-tuple-element.55), channel_id=1, source_target_pairs={{0,16},{8,24},{16,0},{24,8},{1,17},{9,25},{17,1},{25,9},{2,18},{10... | collective-permute-start | bytes 405512 | tf_op jit(solution)/shard_map/ppermute | solution.py:40
  28.1 2.2 %collective-permute-start.16 = (bf16[528,128]{1,0:T(8,128)(2,1)S(1)}, bf16[528,128]{1,0:T(8,128)(2,1)S(1)}, u32[]{:S(2)}, u32[]{:S(2)}) collective-permute-start(bf16[528,128]{1,0:T(8,128)(2,1)S(1)} %get-tuple-element.56), channel_id=1, source_target_pairs={{0,24},{8,16},{16,8},{24,0},{1,25},{9,17},{17,9},{25,1},{2,26},{10... | collective-permute-start | bytes 405512 | tf_op jit(solution)/shard_map/ppermute | solution.py:40
  30.4 1.8 %collective-permute-start.11 = (bf16[528,128]{1,0:T(8,128)(2,1)S(1)}, bf16[528,128]{1,0:T(8,128)(2,1)S(1)}, u32[]{:S(2)}, u32[]{:S(2)}) collective-permute-start(bf16[528,128]{1,0:T(8,128)(2,1)S(1)} %get-tuple-element.51), channel_id=1, source_target_pairs={{0,6},{1,7},{2,4},{3,5},{4,2},{5,3},{6,0},{7,1},{8,14},{9,15},{10,... | collective-permute-start | bytes 405512 | tf_op jit(solution)/shard_map/ppermute | solution.py:40
  32.2 1.2 %collective-permute-start.12 = (bf16[528,128]{1,0:T(8,128)(2,1)S(1)}, bf16[528,128]{1,0:T(8,128)(2,1)S(1)}, u32[]{:S(2)}, u32[]{:S(2)}) collective-permute-start(bf16[528,128]{1,0:T(8,128)(2,1)S(1)} %get-tuple-element.52), channel_id=1, source_target_pairs={{0,4},{1,5},{2,6},{3,7},{4,0},{5,1},{6,2},{7,3},{8,12},{9,13},{10,... | collective-permute-start | bytes 405512 | tf_op jit(solution)/shard_map/ppermute | solution.py:40
  34.1 1.2 %collective-permute-start.13 = (bf16[528,128]{1,0:T(8,128)(2,1)S(1)}, bf16[528,128]{1,0:T(8,128)(2,1)S(1)}, u32[]{:S(2)}, u32[]{:S(2)}) collective-permute-start(bf16[528,128]{1,0:T(8,128)(2,1)S(1)} %get-tuple-element.53), channel_id=1, source_target_pairs={{0,2},{1,3},{2,0},{3,1},{4,6},{5,7},{6,4},{7,5},{8,10},{9,11},{10,... | collective-permute-start | bytes 405512 | tf_op jit(solution)/shard_map/ppermute | solution.py:40
  35.3 4.2 %collective-permute-done.15.refs_8_ = bf16[528,128]{1,0:T(8,128)(2,1)S(1)} collective-permute-done((bf16[528,128]{1,0:T(8,128)(2,1)S(1)}, bf16[528,128]{1,0:T(8,128)(2,1)S(1)}, u32[]{:S(2)}, u32[]{:S(2)}) %collective-permute-start.15) | collective-permute-done | bytes 135200 | tf_op jit(solution)/shard_map/ppermute | solution.py:40
  39.8 3.8 %collective-permute-start.22 = (bf16[8,64,128]{2,1,0:T(8,128)(2,1)S(1)}, bf16[8,64,128]{2,1,0:T(8,128)(2,1)S(1)}, u32[]{:S(2)}, u32[]{:S(2)}) collective-permute-start(bf16[8,64,128]{2,1,0:T(8,128)(2,1)S(1)} %get-tuple-element.59.refs_2_.refs_3_), channel_id=1, source_target_pairs={{0,16},{8,24},{16,0},{24,8},{1,17},{9,25},{17,1},{25,9},{2,18},{10... | collective-permute-start | bytes 393224 | tf_op jit(solution)/shard_map/ppermute | solution.py:40
  43.7 1.9 %collective-permute-start.17 = (bf16[8,64,128]{2,1,0:T(8,128)(2,1)S(1)}, bf16[8,64,128]{2,1,0:T(8,128)(2,1)S(1)}, u32[]{:S(2)}, u32[]{:S(2)}) collective-permute-start(bf16[8,64,128]{2,1,0:T(8,128)(2,1)S(1)} %get-tuple-element.59.refs_2_.refs_3_), channel_id=1, source_target_pairs={{0,6},{1,7},{2,4},{3,5},{4,2},{5,3},{6,0},{7,1},{8,14},{9,15},{10,... | collective-permute-start | bytes 393224 | tf_op jit(solution)/shard_map/ppermute | solution.py:40
  46.2 4.7 %collective-permute-done.20.refs_5_ = bf16[7,64,128]{2,1,0:T(8,128)(2,1)S(1)} collective-permute-done((bf16[7,64,128]{2,1,0:T(8,128)(2,1)S(1)}, bf16[7,64,128]{2,1,0:T(8,128)(2,1)S(1)}, u32[]{:S(2)}, u32[]{:S(2)}) %collective-permute-start.20) | collective-permute-done | bytes 114720 | tf_op jit(solution)/shard_map/ppermute | solution.py:40
  51.2 2.1 %collective-permute-start.26 = (bf16[9,64,128]{2,1,0:T(8,128)(2,1)S(1)}, bf16[9,64,128]{2,1,0:T(8,128)(2,1)S(1)}, u32[]{:S(2)}, u32[]{:S(2)}) collective-permute-start(bf16[9,64,128]{2,1,0:T(8,128)(2,1)S(1)} %pad_maximum_fusion.1), channel_id=1, source_target_pairs={{0,8},{8,0},{16,24},{24,16},{1,9},{9,1},{17,25},{25,17},{2,10},{10... | collective-permute-start | bytes 442376 | tf_op jit(solution)/shard_map/ppermute | solution.py:40
  53.8 2.1 %collective-permute-done.19.refs_5_ = bf16[8,64,128]{2,1,0:T(8,128)(2,1)S(1)} collective-permute-done((bf16[8,64,128]{2,1,0:T(8,128)(2,1)S(1)}, bf16[8,64,128]{2,1,0:T(8,128)(2,1)S(1)}, u32[]{:S(2)}, u32[]{:S(2)}) %collective-permute-start.19) | collective-permute-done | bytes 131104 | tf_op jit(solution)/shard_map/ppermute | solution.py:40
  55.9 1.3 %collective-permute-done.25.refs_9_ = bf16[8,64,128]{2,1,0:T(8,128)(2,1)S(1)} collective-permute-done((bf16[8,64,128]{2,1,0:T(8,128)(2,1)S(1)}, bf16[8,64,128]{2,1,0:T(8,128)(2,1)S(1)}, u32[]{:S(2)}, u32[]{:S(2)}) %collective-permute-start.25) | collective-permute-done | bytes 131104 | tf_op jit(solution)/shard_map/ppermute | solution.py:40
  57.2 1.1 shard_map.67
  58.3 1.4 %shard_map.68 = (f32[64,64,128]{2,1,0:T(8,128)S(1)}, bf16[4,512,128]{2,1,0:T(8,128)(2,1)S(1)}) custom-call(f32[8,64,128]{2,1,0:T(8,128)S(1)} %get-tuple-element.63.refs_0_.refs_4_, s32[3,32]{1,0:T(4,128)S(1)} %copy-done.5, bf16[32,128,128]{2,1,0:T(8,128)(2,1)S(1)} %bitcast.8, ...), custom_call_target="tpu_custom_call", output_to_operand_aliasing={{0}: (7, {})} | custom-call | flops 67108864 | bytes 3670400 | tf_op jit(solution)/shard_map/pallas_call | solution.py:26
  60.0 1.2 %collective-permute-start.31 = (bf16[512,128]{1,0:T(8,128)(2,1)S(1)}, bf16[512,128]{1,0:T(8,128)(2,1)S(1)}, u32[]{:S(2)}, u32[]{:S(2)}) collective-permute-start(bf16[512,128]{1,0:T(8,128)(2,1)S(1)} %get-tuple-element.72), channel_id=1, source_target_pairs={{0,8},{8,0},{16,24},{24,16},{1,9},{9,1},{17,25},{25,17},{2,10},{10... | collective-permute-start | bytes 393224 | tf_op jit(solution)/shard_map/ppermute | solution.py:40
  61.2 3.2 %collective-permute-start.33 = (bf16[512,128]{1,0:T(8,128)(2,1)S(1)}, bf16[512,128]{1,0:T(8,128)(2,1)S(1)}, u32[]{:S(2)}, u32[]{:S(2)}) collective-permute-start(bf16[512,128]{1,0:T(8,128)(2,1)S(1)} %get-tuple-element.74), channel_id=1, source_target_pairs={{0,24},{8,16},{16,8},{24,0},{1,25},{9,17},{17,9},{25,1},{2,26},{10... | collective-permute-start | bytes 393224 | tf_op jit(solution)/shard_map/ppermute | solution.py:40
  64.5 1.1 collective-permute-start.28
  66.2 0.9 collective-permute-done.31.refs_8_
  67.0 1.0 collective-permute-start.30
  68.0 5.9 %collective-permute-done.32.refs_9_ = bf16[512,128]{1,0:T(8,128)(2,1)S(1)} collective-permute-done((bf16[512,128]{1,0:T(8,128)(2,1)S(1)}, bf16[512,128]{1,0:T(8,128)(2,1)S(1)}, u32[]{:S(2)}, u32[]{:S(2)}) %collective-permute-start.32) | collective-permute-done | bytes 131104 | tf_op jit(solution)/shard_map/ppermute | solution.py:40
  74.2 2.3 %collective-permute-start.39 = (bf16[8,64,128]{2,1,0:T(8,128)(2,1)S(1)}, bf16[8,64,128]{2,1,0:T(8,128)(2,1)S(1)}, u32[]{:S(2)}, u32[]{:S(2)}) collective-permute-start(bf16[8,64,128]{2,1,0:T(8,128)(2,1)S(1)} %get-tuple-element.76.refs_2_.refs_3_), channel_id=1, source_target_pairs={{0,16},{8,24},{16,0},{24,8},{1,17},{9,25},{17,1},{25,9},{2,18},{10... | collective-permute-start | bytes 393224 | tf_op jit(solution)/shard_map/ppermute | solution.py:40
  77.0 1.8 %collective-permute-start.34 = (bf16[8,64,128]{2,1,0:T(8,128)(2,1)S(1)}, bf16[8,64,128]{2,1,0:T(8,128)(2,1)S(1)}, u32[]{:S(2)}, u32[]{:S(2)}) collective-permute-start(bf16[8,64,128]{2,1,0:T(8,128)(2,1)S(1)} %get-tuple-element.76.refs_2_.refs_3_), channel_id=1, source_target_pairs={{0,6},{1,7},{2,4},{3,5},{4,2},{5,3},{6,0},{7,1},{8,14},{9,15},{10,... | collective-permute-start | bytes 393224 | tf_op jit(solution)/shard_map/ppermute | solution.py:40
  79.7 3.2 %collective-permute-done.37.refs_5_ = bf16[7,64,128]{2,1,0:T(8,128)(2,1)S(1)} collective-permute-done((bf16[7,64,128]{2,1,0:T(8,128)(2,1)S(1)}, bf16[7,64,128]{2,1,0:T(8,128)(2,1)S(1)}, u32[]{:S(2)}, u32[]{:S(2)}) %collective-permute-start.37) | collective-permute-done | bytes 114720 | tf_op jit(solution)/shard_map/ppermute | solution.py:40
  82.9 1.0 collective-permute-start.36
  84.6 2.5 %collective-permute-start.43 = (bf16[9,64,128]{2,1,0:T(8,128)(2,1)S(1)}, bf16[9,64,128]{2,1,0:T(8,128)(2,1)S(1)}, u32[]{:S(2)}, u32[]{:S(2)}) collective-permute-start(bf16[9,64,128]{2,1,0:T(8,128)(2,1)S(1)} %pad_maximum_fusion.2), channel_id=1, source_target_pairs={{0,8},{8,0},{16,24},{24,16},{1,9},{9,1},{17,25},{25,17},{2,10},{10... | collective-permute-start | bytes 442376 | tf_op jit(solution)/shard_map/ppermute | solution.py:40
  88.7 1.0 collective-permute-done.42.refs_9_
  89.7 1.0 shard_map.72.refs_1_
  90.7 1.2 %shard_map.73 = f32[40,128]{1,0:T(8,128)S(1)} custom-call(s32[3,32]{1,0:T(4,128)S(1)} %copy-done.5, bf16[64,4096]{1,0:T(8,128)(2,1)S(1)} %shard_map.72.refs_1_, f32[64,128]{1,0:T(8,128)S(1)} %shard_map.71.refs_2_, bf16[8,64,128]{2,1,0:T(8,128)(2,1)S(1)} %get-tuple-element.76.refs_2_.refs_3_, bf16[8,64,128]{2,1,0:T(8,128)(2,1)S(1)} %collective-permute-done.39.refs_4_, ...), custom_call_target="tpu_custom_call" | custom-call | flops 33554432 | bytes 1081728 | tf_op jit(solution)/shard_map/pallas_call | solution.py:26
  92.1 1.0 collective-permute-done.44
  93.1 1.8 %collective-permute-start.45 = (f32[40,128]{1,0:T(8,128)S(1)}, f32[40,128]{1,0:T(8,128)S(1)}, u32[]{:S(2)}, u32[]{:S(2)}) collective-permute-start(f32[40,128]{1,0:T(8,128)S(1)} %add.12), channel_id=1, source_target_pairs={{0,6},{1,7},{2,4},{3,5},{4,2},{5,3},{6,0},{7,1},{8,14},{9,15},{10,... | collective-permute-start | bytes 61448 | tf_op jit(solution)/shard_map/ppermute | solution.py:40
  95.3 1.3 %collective-permute-start.47 = (f32[40,128]{1,0:T(8,128)S(1)}, f32[40,128]{1,0:T(8,128)S(1)}, u32[]{:S(2)}, u32[]{:S(2)}) collective-permute-start(f32[40,128]{1,0:T(8,128)S(1)} %add.12), channel_id=1, source_target_pairs={{0,2},{1,3},{2,0},{3,1},{4,6},{5,7},{6,4},{7,5},{8,10},{9,11},{10,... | collective-permute-start | bytes 61448 | tf_op jit(solution)/shard_map/ppermute | solution.py:40
  96.6 1.3 %collective-permute-done.45 = f32[40,128]{1,0:T(8,128)S(1)} collective-permute-done((f32[40,128]{1,0:T(8,128)S(1)}, f32[40,128]{1,0:T(8,128)S(1)}, u32[]{:S(2)}, u32[]{:S(2)}) %collective-permute-start.45) | collective-permute-done | bytes 20512 | tf_op jit(solution)/shard_map/ppermute | solution.py:40
  99.1 3.1 %collective-permute-start.48 = (f32[40,128]{1,0:T(8,128)S(1)}, f32[40,128]{1,0:T(8,128)S(1)}, u32[]{:S(2)}, u32[]{:S(2)}) collective-permute-start(f32[40,128]{1,0:T(8,128)S(1)} %add_add_fusion.refs_1_), channel_id=1, source_target_pairs={{0,24},{8,16},{16,8},{24,0},{1,25},{9,17},{17,9},{25,1},{2,26},{10... | collective-permute-start | bytes 61448 | tf_op jit(solution)/shard_map/ppermute | solution.py:40
  102.2 0.9 collective-permute-start.49
  103.6 1.2 %collective-permute-done.48.refs_2_ = f32[40,128]{1,0:T(8,128)S(1)} collective-permute-done((f32[40,128]{1,0:T(8,128)S(1)}, f32[40,128]{1,0:T(8,128)S(1)}, u32[]{:S(2)}, u32[]{:S(2)}) %collective-permute-start.48) | collective-permute-done | bytes 20512 | tf_op jit(solution)/shard_map/ppermute | solution.py:40
  104.8 2.2 %collective-permute-done.49.refs_3_ = f32[40,128]{1,0:T(8,128)S(1)} collective-permute-done((f32[40,128]{1,0:T(8,128)S(1)}, f32[40,128]{1,0:T(8,128)S(1)}, u32[]{:S(2)}, u32[]{:S(2)}) %collective-permute-start.49) | collective-permute-done | bytes 20512 | tf_op jit(solution)/shard_map/ppermute | solution.py:40
  107.1 3.8 %shard_map.74 = (f32[64,1024]{1,0:T(8,128)}, f32[64,64]{1,0:T(8,128)}) custom-call(f32[64,1024]{1,0:T(8,128)S(1)} %get-tuple-element.75.refs_0_, f32[40,128]{1,0:T(8,128)S(1)} %add_add_fusion.refs_1_, f32[40,128]{1,0:T(8,128)S(1)} %collective-permute-done.48.refs_2_, f32[40,128]{1,0:T(8,128)S(1)} %collective-permute-done.49.refs_3_, ...), custom_call_target="tpu_custom_call" | custom-call | bytes 344064 | tf_op jit(solution)/shard_map/pallas_call | solution.py:26
  (94 shorter events, 15.6 us)
Async XLA Ops:
  3.2 8.6 %collective-permute-start.3 = (bf16[7,64,128]{2,1,0:T(8,128)(2,1)S(1)}, bf16[7,64,128]{2,1,0:T(8,128)(2,1)S(1)}, u32[]{:S(2)}, u32[]{:S(2)}) collective-permute-start(bf16[7,64,128]{2,1,0:T(8,128)(2,1)S(1)} %slice.24), channel_id=1, source_target_pairs={{0,8},{8,0},{16,24},{24,16},{1,9},{9,1},{17,25},{25,17},{2,10},{10... | collective-permute-start | bytes 344072 | tf_op jit(solution)/shard_map/ppermute | solution.py:40
  6.3 9.6 %collective-permute-start.4 = (bf16[8,64,128]{2,1,0:T(8,128)(2,1)}, bf16[8,64,128]{2,1,0:T(8,128)(2,1)S(1)}, u32[]{:S(2)}, u32[]{:S(2)}) collective-permute-start(bf16[8,64,128]{2,1,0:T(8,128)(2,1)} %shard_map.60.refs_2_.refs_3_), channel_id=1, source_target_pairs={{0,1},{1,0},{2,3},{3,2},{4,5},{5,4},{6,7},{7,6},{8,9},{9,8},{10,11... | collective-permute-start | bytes 393224 | tf_op jit(solution)/shard_map/ppermute | solution.py:40
  6.3 9.8 %collective-permute-start.5 = (bf16[8,64,128]{2,1,0:T(8,128)(2,1)}, bf16[8,64,128]{2,1,0:T(8,128)(2,1)S(1)}, u32[]{:S(2)}, u32[]{:S(2)}) collective-permute-start(bf16[8,64,128]{2,1,0:T(8,128)(2,1)} %shard_map.60.refs_2_.refs_3_), channel_id=1, source_target_pairs={{0,16},{8,24},{16,0},{24,8},{1,17},{9,25},{17,1},{25,9},{2,18},{10... | collective-permute-start | bytes 393224 | tf_op jit(solution)/shard_map/ppermute | solution.py:40
  8.9 7.5 %collective-permute-start = (bf16[8,64,128]{2,1,0:T(8,128)(2,1)}, bf16[8,64,128]{2,1,0:T(8,128)(2,1)S(1)}, u32[]{:S(2)}, u32[]{:S(2)}) collective-permute-start(bf16[8,64,128]{2,1,0:T(8,128)(2,1)} %shard_map.60.refs_2_.refs_3_), channel_id=1, source_target_pairs={{0,6},{1,7},{2,4},{3,5},{4,2},{5,3},{6,0},{7,1},{8,14},{9,15},{10,... | collective-permute-start | bytes 393224 | tf_op jit(solution)/shard_map/ppermute | solution.py:40
  11.3 7.1 %collective-permute-start.1 = (bf16[8,64,128]{2,1,0:T(8,128)(2,1)}, bf16[8,64,128]{2,1,0:T(8,128)(2,1)S(1)}, u32[]{:S(2)}, u32[]{:S(2)}) collective-permute-start(bf16[8,64,128]{2,1,0:T(8,128)(2,1)} %shard_map.60.refs_2_.refs_3_), channel_id=1, source_target_pairs={{0,4},{1,5},{2,6},{3,7},{4,0},{5,1},{6,2},{7,3},{8,12},{9,13},{10,... | collective-permute-start | bytes 393224 | tf_op jit(solution)/shard_map/ppermute | solution.py:40
  11.8 6.7 %collective-permute-start.2 = (bf16[8,64,128]{2,1,0:T(8,128)(2,1)}, bf16[8,64,128]{2,1,0:T(8,128)(2,1)S(1)}, u32[]{:S(2)}, u32[]{:S(2)}) collective-permute-start(bf16[8,64,128]{2,1,0:T(8,128)(2,1)} %shard_map.60.refs_2_.refs_3_), channel_id=1, source_target_pairs={{0,2},{1,3},{2,0},{3,1},{4,6},{5,7},{6,4},{7,5},{8,10},{9,11},{10,... | collective-permute-start | bytes 393224 | tf_op jit(solution)/shard_map/ppermute | solution.py:40
  16.1 7.9 %collective-permute-start.9 = (bf16[9,64,128]{2,1,0:T(8,128)(2,1)S(1)}, bf16[9,64,128]{2,1,0:T(8,128)(2,1)S(1)}, u32[]{:S(2)}, u32[]{:S(2)}) collective-permute-start(bf16[9,64,128]{2,1,0:T(8,128)(2,1)S(1)} %pad_maximum_fusion), channel_id=1, source_target_pairs={{0,8},{8,0},{16,24},{24,16},{1,9},{9,1},{17,25},{25,17},{2,10},{10... | collective-permute-start | bytes 442376 | tf_op jit(solution)/shard_map/ppermute | solution.py:40
  16.4 2.5 %collective-permute-start.6 = (bf16[8,64,128]{2,1,0:T(8,128)(2,1)S(1)}, bf16[8,64,128]{2,1,0:T(8,128)(2,1)S(1)}, u32[]{:S(2)}, u32[]{:S(2)}) collective-permute-start(bf16[8,64,128]{2,1,0:T(8,128)(2,1)S(1)} %collective-permute-done.refs_3_), channel_id=1, source_target_pairs={{0,1},{1,0},{2,3},{3,2},{4,5},{5,4},{6,7},{7,6},{8,9},{9,8},{10,11... | collective-permute-start | bytes 393224 | tf_op jit(solution)/shard_map/ppermute | solution.py:40
  18.4 1.3 %collective-permute-start.7 = (bf16[8,64,128]{2,1,0:T(8,128)(2,1)S(1)}, bf16[8,64,128]{2,1,0:T(8,128)(2,1)S(1)}, u32[]{:S(2)}, u32[]{:S(2)}) collective-permute-start(bf16[8,64,128]{2,1,0:T(8,128)(2,1)S(1)} %collective-permute-done.1.refs_4_), channel_id=1, source_target_pairs={{0,1},{1,0},{2,3},{3,2},{4,5},{5,4},{6,7},{7,6},{8,9},{9,8},{10,11... | collective-permute-start | bytes 393224 | tf_op jit(solution)/shard_map/ppermute | solution.py:40
  18.5 1.4 %collective-permute-start.8 = (bf16[8,64,128]{2,1,0:T(8,128)(2,1)S(1)}, bf16[8,64,128]{2,1,0:T(8,128)(2,1)S(1)}, u32[]{:S(2)}, u32[]{:S(2)}) collective-permute-start(bf16[8,64,128]{2,1,0:T(8,128)(2,1)S(1)} %collective-permute-done.2.refs_5_), channel_id=1, source_target_pairs={{0,1},{1,0},{2,3},{3,2},{4,5},{5,4},{6,7},{7,6},{8,9},{9,8},{10,11... | collective-permute-start | bytes 393224 | tf_op jit(solution)/shard_map/ppermute | solution.py:40
  25.5 4.8 %collective-permute-start.10 = (bf16[4,528,128]{2,1,0:T(8,128)(2,1)S(1)}, bf16[4,528,128]{2,1,0:T(8,128)(2,1)S(1)}, u32[]{:S(2)}, u32[]{:S(2)}) collective-permute-start(bf16[4,528,128]{2,1,0:T(8,128)(2,1)S(1)} %get-tuple-element.48), channel_id=1, source_target_pairs={{0,1},{1,0},{2,3},{3,2},{4,5},{5,4},{6,7},{7,6},{8,9},{9,8},{10,11... | collective-permute-start | bytes 1622024 | tf_op jit(solution)/shard_map/ppermute | solution.py:40
  25.9 8.2 %collective-permute-start.14 = (bf16[528,128]{1,0:T(8,128)(2,1)S(1)}, bf16[528,128]{1,0:T(8,128)(2,1)S(1)}, u32[]{:S(2)}, u32[]{:S(2)}) collective-permute-start(bf16[528,128]{1,0:T(8,128)(2,1)S(1)} %get-tuple-element.54), channel_id=1, source_target_pairs={{0,8},{8,0},{16,24},{24,16},{1,9},{9,1},{17,25},{25,17},{2,10},{10... | collective-permute-start | bytes 405512 | tf_op jit(solution)/shard_map/ppermute | solution.py:40
  26.4 13.2 %collective-permute-start.15 = (bf16[528,128]{1,0:T(8,128)(2,1)S(1)}, bf16[528,128]{1,0:T(8,128)(2,1)S(1)}, u32[]{:S(2)}, u32[]{:S(2)}) collective-permute-start(bf16[528,128]{1,0:T(8,128)(2,1)S(1)} %get-tuple-element.55), channel_id=1, source_target_pairs={{0,16},{8,24},{16,0},{24,8},{1,17},{9,25},{17,1},{25,9},{2,18},{10... | collective-permute-start | bytes 405512 | tf_op jit(solution)/shard_map/ppermute | solution.py:40
  28.1 11.4 %collective-permute-start.16 = (bf16[528,128]{1,0:T(8,128)(2,1)S(1)}, bf16[528,128]{1,0:T(8,128)(2,1)S(1)}, u32[]{:S(2)}, u32[]{:S(2)}) collective-permute-start(bf16[528,128]{1,0:T(8,128)(2,1)S(1)} %get-tuple-element.56), channel_id=1, source_target_pairs={{0,24},{8,16},{16,8},{24,0},{1,25},{9,17},{17,9},{25,1},{2,26},{10... | collective-permute-start | bytes 405512 | tf_op jit(solution)/shard_map/ppermute | solution.py:40
  30.4 9.1 %collective-permute-start.11 = (bf16[528,128]{1,0:T(8,128)(2,1)S(1)}, bf16[528,128]{1,0:T(8,128)(2,1)S(1)}, u32[]{:S(2)}, u32[]{:S(2)}) collective-permute-start(bf16[528,128]{1,0:T(8,128)(2,1)S(1)} %get-tuple-element.51), channel_id=1, source_target_pairs={{0,6},{1,7},{2,4},{3,5},{4,2},{5,3},{6,0},{7,1},{8,14},{9,15},{10,... | collective-permute-start | bytes 405512 | tf_op jit(solution)/shard_map/ppermute | solution.py:40
  32.2 7.3 %collective-permute-start.12 = (bf16[528,128]{1,0:T(8,128)(2,1)S(1)}, bf16[528,128]{1,0:T(8,128)(2,1)S(1)}, u32[]{:S(2)}, u32[]{:S(2)}) collective-permute-start(bf16[528,128]{1,0:T(8,128)(2,1)S(1)} %get-tuple-element.52), channel_id=1, source_target_pairs={{0,4},{1,5},{2,6},{3,7},{4,0},{5,1},{6,2},{7,3},{8,12},{9,13},{10,... | collective-permute-start | bytes 405512 | tf_op jit(solution)/shard_map/ppermute | solution.py:40
  34.1 5.4 %collective-permute-start.13 = (bf16[528,128]{1,0:T(8,128)(2,1)S(1)}, bf16[528,128]{1,0:T(8,128)(2,1)S(1)}, u32[]{:S(2)}, u32[]{:S(2)}) collective-permute-start(bf16[528,128]{1,0:T(8,128)(2,1)S(1)} %get-tuple-element.53), channel_id=1, source_target_pairs={{0,2},{1,3},{2,0},{3,1},{4,6},{5,7},{6,4},{7,5},{8,10},{9,11},{10,... | collective-permute-start | bytes 405512 | tf_op jit(solution)/shard_map/ppermute | solution.py:40
  39.7 11.4 %collective-permute-start.21 = (bf16[8,64,128]{2,1,0:T(8,128)(2,1)S(1)}, bf16[8,64,128]{2,1,0:T(8,128)(2,1)S(1)}, u32[]{:S(2)}, u32[]{:S(2)}) collective-permute-start(bf16[8,64,128]{2,1,0:T(8,128)(2,1)S(1)} %get-tuple-element.59.refs_2_.refs_3_), channel_id=1, source_target_pairs={{0,1},{1,0},{2,3},{3,2},{4,5},{5,4},{6,7},{7,6},{8,9},{9,8},{10,11... | collective-permute-start | bytes 393224 | tf_op jit(solution)/shard_map/ppermute | solution.py:40
  39.8 11.3 %collective-permute-start.22 = (bf16[8,64,128]{2,1,0:T(8,128)(2,1)S(1)}, bf16[8,64,128]{2,1,0:T(8,128)(2,1)S(1)}, u32[]{:S(2)}, u32[]{:S(2)}) collective-permute-start(bf16[8,64,128]{2,1,0:T(8,128)(2,1)S(1)} %get-tuple-element.59.refs_2_.refs_3_), channel_id=1, source_target_pairs={{0,16},{8,24},{16,0},{24,8},{1,17},{9,25},{17,1},{25,9},{2,18},{10... | collective-permute-start | bytes 393224 | tf_op jit(solution)/shard_map/ppermute | solution.py:40
  43.7 7.2 %collective-permute-start.20 = (bf16[7,64,128]{2,1,0:T(8,128)(2,1)S(1)}, bf16[7,64,128]{2,1,0:T(8,128)(2,1)S(1)}, u32[]{:S(2)}, u32[]{:S(2)}) collective-permute-start(bf16[7,64,128]{2,1,0:T(8,128)(2,1)S(1)} %slice.20), channel_id=1, source_target_pairs={{0,8},{8,0},{16,24},{24,16},{1,9},{9,1},{17,25},{25,17},{2,10},{10... | collective-permute-start | bytes 344072 | tf_op jit(solution)/shard_map/ppermute | solution.py:40
  43.7 9.5 %collective-permute-start.17 = (bf16[8,64,128]{2,1,0:T(8,128)(2,1)S(1)}, bf16[8,64,128]{2,1,0:T(8,128)(2,1)S(1)}, u32[]{:S(2)}, u32[]{:S(2)}) collective-permute-start(bf16[8,64,128]{2,1,0:T(8,128)(2,1)S(1)} %get-tuple-element.59.refs_2_.refs_3_), channel_id=1, source_target_pairs={{0,6},{1,7},{2,4},{3,5},{4,2},{5,3},{6,0},{7,1},{8,14},{9,15},{10,... | collective-permute-start | bytes 393224 | tf_op jit(solution)/shard_map/ppermute | solution.py:40
  45.6 7.6 %collective-permute-start.18 = (bf16[8,64,128]{2,1,0:T(8,128)(2,1)S(1)}, bf16[8,64,128]{2,1,0:T(8,128)(2,1)S(1)}, u32[]{:S(2)}, u32[]{:S(2)}) collective-permute-start(bf16[8,64,128]{2,1,0:T(8,128)(2,1)S(1)} %get-tuple-element.59.refs_2_.refs_3_), channel_id=1, source_target_pairs={{0,4},{1,5},{2,6},{3,7},{4,0},{5,1},{6,2},{7,3},{8,12},{9,13},{10,... | collective-permute-start | bytes 393224 | tf_op jit(solution)/shard_map/ppermute | solution.py:40
  50.9 5.0 %collective-permute-start.19 = (bf16[8,64,128]{2,1,0:T(8,128)(2,1)S(1)}, bf16[8,64,128]{2,1,0:T(8,128)(2,1)S(1)}, u32[]{:S(2)}, u32[]{:S(2)}) collective-permute-start(bf16[8,64,128]{2,1,0:T(8,128)(2,1)S(1)} %get-tuple-element.59.refs_2_.refs_3_), channel_id=1, source_target_pairs={{0,2},{1,3},{2,0},{3,1},{4,6},{5,7},{6,4},{7,5},{8,10},{9,11},{10,... | collective-permute-start | bytes 393224 | tf_op jit(solution)/shard_map/ppermute | solution.py:40
  51.2 7.1 %collective-permute-start.26 = (bf16[9,64,128]{2,1,0:T(8,128)(2,1)S(1)}, bf16[9,64,128]{2,1,0:T(8,128)(2,1)S(1)}, u32[]{:S(2)}, u32[]{:S(2)}) collective-permute-start(bf16[9,64,128]{2,1,0:T(8,128)(2,1)S(1)} %pad_maximum_fusion.1), channel_id=1, source_target_pairs={{0,8},{8,0},{16,24},{24,16},{1,9},{9,1},{17,25},{25,17},{2,10},{10... | collective-permute-start | bytes 442376 | tf_op jit(solution)/shard_map/ppermute | solution.py:40
  53.2 2.6 %collective-permute-start.23 = (bf16[8,64,128]{2,1,0:T(8,128)(2,1)S(1)}, bf16[8,64,128]{2,1,0:T(8,128)(2,1)S(1)}, u32[]{:S(2)}, u32[]{:S(2)}) collective-permute-start(bf16[8,64,128]{2,1,0:T(8,128)(2,1)S(1)} %collective-permute-done.17.refs_3_), channel_id=1, source_target_pairs={{0,1},{1,0},{2,3},{3,2},{4,5},{5,4},{6,7},{7,6},{8,9},{9,8},{10,11... | collective-permute-start | bytes 393224 | tf_op jit(solution)/shard_map/ppermute | solution.py:40
  53.2 2.6 %collective-permute-start.24 = (bf16[8,64,128]{2,1,0:T(8,128)(2,1)S(1)}, bf16[8,64,128]{2,1,0:T(8,128)(2,1)S(1)}, u32[]{:S(2)}, u32[]{:S(2)}) collective-permute-start(bf16[8,64,128]{2,1,0:T(8,128)(2,1)S(1)} %collective-permute-done.18.refs_4_), channel_id=1, source_target_pairs={{0,1},{1,0},{2,3},{3,2},{4,5},{5,4},{6,7},{7,6},{8,9},{9,8},{10,11... | collective-permute-start | bytes 393224 | tf_op jit(solution)/shard_map/ppermute | solution.py:40
  59.8 4.6 %collective-permute-start.27 = (bf16[4,512,128]{2,1,0:T(8,128)(2,1)S(1)}, bf16[4,512,128]{2,1,0:T(8,128)(2,1)S(1)}, u32[]{:S(2)}, u32[]{:S(2)}) collective-permute-start(bf16[4,512,128]{2,1,0:T(8,128)(2,1)S(1)} %get-tuple-element.67), channel_id=1, source_target_pairs={{0,1},{1,0},{2,3},{3,2},{4,5},{5,4},{6,7},{7,6},{8,9},{9,8},{10,11... | collective-permute-start | bytes 1572872 | tf_op jit(solution)/shard_map/ppermute | solution.py:40
  60.0 7.1 %collective-permute-start.31 = (bf16[512,128]{1,0:T(8,128)(2,1)S(1)}, bf16[512,128]{1,0:T(8,128)(2,1)S(1)}, u32[]{:S(2)}, u32[]{:S(2)}) collective-permute-start(bf16[512,128]{1,0:T(8,128)(2,1)S(1)} %get-tuple-element.72), channel_id=1, source_target_pairs={{0,8},{8,0},{16,24},{24,16},{1,9},{9,1},{17,25},{25,17},{2,10},{10... | collective-permute-start | bytes 393224 | tf_op jit(solution)/shard_map/ppermute | solution.py:40
  61.2 12.7 %collective-permute-start.32 = (bf16[512,128]{1,0:T(8,128)(2,1)S(1)}, bf16[512,128]{1,0:T(8,128)(2,1)S(1)}, u32[]{:S(2)}, u32[]{:S(2)}) collective-permute-start(bf16[512,128]{1,0:T(8,128)(2,1)S(1)} %get-tuple-element.73), channel_id=1, source_target_pairs={{0,16},{8,24},{16,0},{24,8},{1,17},{9,25},{17,1},{25,9},{2,18},{10... | collective-permute-start | bytes 393224 | tf_op jit(solution)/shard_map/ppermute | solution.py:40
  61.2 12.7 %collective-permute-start.33 = (bf16[512,128]{1,0:T(8,128)(2,1)S(1)}, bf16[512,128]{1,0:T(8,128)(2,1)S(1)}, u32[]{:S(2)}, u32[]{:S(2)}) collective-permute-start(bf16[512,128]{1,0:T(8,128)(2,1)S(1)} %get-tuple-element.74), channel_id=1, source_target_pairs={{0,24},{8,16},{16,8},{24,0},{1,25},{9,17},{17,9},{25,1},{2,26},{10... | collective-permute-start | bytes 393224 | tf_op jit(solution)/shard_map/ppermute | solution.py:40
  64.5 9.5 %collective-permute-start.28 = (bf16[512,128]{1,0:T(8,128)(2,1)S(1)}, bf16[512,128]{1,0:T(8,128)(2,1)S(1)}, u32[]{:S(2)}, u32[]{:S(2)}) collective-permute-start(bf16[512,128]{1,0:T(8,128)(2,1)S(1)} %get-tuple-element.69), channel_id=1, source_target_pairs={{0,6},{1,7},{2,4},{3,5},{4,2},{5,3},{6,0},{7,1},{8,14},{9,15},{10,... | collective-permute-start | bytes 393224 | tf_op jit(solution)/shard_map/ppermute | solution.py:40
  65.5 8.4 %collective-permute-start.29 = (bf16[512,128]{1,0:T(8,128)(2,1)S(1)}, bf16[512,128]{1,0:T(8,128)(2,1)S(1)}, u32[]{:S(2)}, u32[]{:S(2)}) collective-permute-start(bf16[512,128]{1,0:T(8,128)(2,1)S(1)} %get-tuple-element.70), channel_id=1, source_target_pairs={{0,4},{1,5},{2,6},{3,7},{4,0},{5,1},{6,2},{7,3},{8,12},{9,13},{10,... | collective-permute-start | bytes 393224 | tf_op jit(solution)/shard_map/ppermute | solution.py:40
  67.0 6.9 %collective-permute-start.30 = (bf16[512,128]{1,0:T(8,128)(2,1)S(1)}, bf16[512,128]{1,0:T(8,128)(2,1)S(1)}, u32[]{:S(2)}, u32[]{:S(2)}) collective-permute-start(bf16[512,128]{1,0:T(8,128)(2,1)S(1)} %get-tuple-element.71), channel_id=1, source_target_pairs={{0,2},{1,3},{2,0},{3,1},{4,6},{5,7},{6,4},{7,5},{8,10},{9,11},{10,... | collective-permute-start | bytes 393224 | tf_op jit(solution)/shard_map/ppermute | solution.py:40
  74.2 10.4 %collective-permute-start.38 = (bf16[8,64,128]{2,1,0:T(8,128)(2,1)S(1)}, bf16[8,64,128]{2,1,0:T(8,128)(2,1)S(1)}, u32[]{:S(2)}, u32[]{:S(2)}) collective-permute-start(bf16[8,64,128]{2,1,0:T(8,128)(2,1)S(1)} %get-tuple-element.76.refs_2_.refs_3_), channel_id=1, source_target_pairs={{0,1},{1,0},{2,3},{3,2},{4,5},{5,4},{6,7},{7,6},{8,9},{9,8},{10,11... | collective-permute-start | bytes 393224 | tf_op jit(solution)/shard_map/ppermute | solution.py:40
  74.2 10.3 %collective-permute-start.39 = (bf16[8,64,128]{2,1,0:T(8,128)(2,1)S(1)}, bf16[8,64,128]{2,1,0:T(8,128)(2,1)S(1)}, u32[]{:S(2)}, u32[]{:S(2)}) collective-permute-start(bf16[8,64,128]{2,1,0:T(8,128)(2,1)S(1)} %get-tuple-element.76.refs_2_.refs_3_), channel_id=1, source_target_pairs={{0,16},{8,24},{16,0},{24,8},{1,17},{9,25},{17,1},{25,9},{2,18},{10... | collective-permute-start | bytes 393224 | tf_op jit(solution)/shard_map/ppermute | solution.py:40
  76.5 6.4 %collective-permute-start.37 = (bf16[7,64,128]{2,1,0:T(8,128)(2,1)S(1)}, bf16[7,64,128]{2,1,0:T(8,128)(2,1)S(1)}, u32[]{:S(2)}, u32[]{:S(2)}) collective-permute-start(bf16[7,64,128]{2,1,0:T(8,128)(2,1)S(1)} %slice.22), channel_id=1, source_target_pairs={{0,8},{8,0},{16,24},{24,16},{1,9},{9,1},{17,25},{25,17},{2,10},{10... | collective-permute-start | bytes 344072 | tf_op jit(solution)/shard_map/ppermute | solution.py:40
  77.0 10.1 %collective-permute-start.34 = (bf16[8,64,128]{2,1,0:T(8,128)(2,1)S(1)}, bf16[8,64,128]{2,1,0:T(8,128)(2,1)S(1)}, u32[]{:S(2)}, u32[]{:S(2)}) collective-permute-start(bf16[8,64,128]{2,1,0:T(8,128)(2,1)S(1)} %get-tuple-element.76.refs_2_.refs_3_), channel_id=1, source_target_pairs={{0,6},{1,7},{2,4},{3,5},{4,2},{5,3},{6,0},{7,1},{8,14},{9,15},{10,... | collective-permute-start | bytes 393224 | tf_op jit(solution)/shard_map/ppermute | solution.py:40
  78.9 8.3 %collective-permute-start.35 = (bf16[8,64,128]{2,1,0:T(8,128)(2,1)S(1)}, bf16[8,64,128]{2,1,0:T(8,128)(2,1)S(1)}, u32[]{:S(2)}, u32[]{:S(2)}) collective-permute-start(bf16[8,64,128]{2,1,0:T(8,128)(2,1)S(1)} %get-tuple-element.76.refs_2_.refs_3_), channel_id=1, source_target_pairs={{0,4},{1,5},{2,6},{3,7},{4,0},{5,1},{6,2},{7,3},{8,12},{9,13},{10,... | collective-permute-start | bytes 393224 | tf_op jit(solution)/shard_map/ppermute | solution.py:40
  82.9 5.4 %collective-permute-start.36 = (bf16[8,64,128]{2,1,0:T(8,128)(2,1)S(1)}, bf16[8,64,128]{2,1,0:T(8,128)(2,1)S(1)}, u32[]{:S(2)}, u32[]{:S(2)}) collective-permute-start(bf16[8,64,128]{2,1,0:T(8,128)(2,1)S(1)} %get-tuple-element.76.refs_2_.refs_3_), channel_id=1, source_target_pairs={{0,2},{1,3},{2,0},{3,1},{4,6},{5,7},{6,4},{7,5},{8,10},{9,11},{10,... | collective-permute-start | bytes 393224 | tf_op jit(solution)/shard_map/ppermute | solution.py:40
  84.6 6.1 %collective-permute-start.43 = (bf16[9,64,128]{2,1,0:T(8,128)(2,1)S(1)}, bf16[9,64,128]{2,1,0:T(8,128)(2,1)S(1)}, u32[]{:S(2)}, u32[]{:S(2)}) collective-permute-start(bf16[9,64,128]{2,1,0:T(8,128)(2,1)S(1)} %pad_maximum_fusion.2), channel_id=1, source_target_pairs={{0,8},{8,0},{16,24},{24,16},{1,9},{9,1},{17,25},{25,17},{2,10},{10... | collective-permute-start | bytes 442376 | tf_op jit(solution)/shard_map/ppermute | solution.py:40
  87.2 1.3 %collective-permute-start.40 = (bf16[8,64,128]{2,1,0:T(8,128)(2,1)S(1)}, bf16[8,64,128]{2,1,0:T(8,128)(2,1)S(1)}, u32[]{:S(2)}, u32[]{:S(2)}) collective-permute-start(bf16[8,64,128]{2,1,0:T(8,128)(2,1)S(1)} %collective-permute-done.34.refs_3_), channel_id=1, source_target_pairs={{0,1},{1,0},{2,3},{3,2},{4,5},{5,4},{6,7},{7,6},{8,9},{9,8},{10,11... | collective-permute-start | bytes 393224 | tf_op jit(solution)/shard_map/ppermute | solution.py:40
  87.2 1.5 %collective-permute-start.41 = (bf16[8,64,128]{2,1,0:T(8,128)(2,1)S(1)}, bf16[8,64,128]{2,1,0:T(8,128)(2,1)S(1)}, u32[]{:S(2)}, u32[]{:S(2)}) collective-permute-start(bf16[8,64,128]{2,1,0:T(8,128)(2,1)S(1)} %collective-permute-done.35.refs_4_), channel_id=1, source_target_pairs={{0,1},{1,0},{2,3},{3,2},{4,5},{5,4},{6,7},{7,6},{8,9},{9,8},{10,11... | collective-permute-start | bytes 393224 | tf_op jit(solution)/shard_map/ppermute | solution.py:40
  93.1 4.7 %collective-permute-start.45 = (f32[40,128]{1,0:T(8,128)S(1)}, f32[40,128]{1,0:T(8,128)S(1)}, u32[]{:S(2)}, u32[]{:S(2)}) collective-permute-start(f32[40,128]{1,0:T(8,128)S(1)} %add.12), channel_id=1, source_target_pairs={{0,6},{1,7},{2,4},{3,5},{4,2},{5,3},{6,0},{7,1},{8,14},{9,15},{10,... | collective-permute-start | bytes 61448 | tf_op jit(solution)/shard_map/ppermute | solution.py:40
  95.0 3.8 %collective-permute-start.46 = (f32[40,128]{1,0:T(8,128)S(1)}, f32[40,128]{1,0:T(8,128)S(1)}, u32[]{:S(2)}, u32[]{:S(2)}) collective-permute-start(f32[40,128]{1,0:T(8,128)S(1)} %add.12), channel_id=1, source_target_pairs={{0,4},{1,5},{2,6},{3,7},{4,0},{5,1},{6,2},{7,3},{8,12},{9,13},{10,... | collective-permute-start | bytes 61448 | tf_op jit(solution)/shard_map/ppermute | solution.py:40
  95.3 3.8 %collective-permute-start.47 = (f32[40,128]{1,0:T(8,128)S(1)}, f32[40,128]{1,0:T(8,128)S(1)}, u32[]{:S(2)}, u32[]{:S(2)}) collective-permute-start(f32[40,128]{1,0:T(8,128)S(1)} %add.12), channel_id=1, source_target_pairs={{0,2},{1,3},{2,0},{3,1},{4,6},{5,7},{6,4},{7,5},{8,10},{9,11},{10,... | collective-permute-start | bytes 61448 | tf_op jit(solution)/shard_map/ppermute | solution.py:40
  99.1 5.6 %collective-permute-start.48 = (f32[40,128]{1,0:T(8,128)S(1)}, f32[40,128]{1,0:T(8,128)S(1)}, u32[]{:S(2)}, u32[]{:S(2)}) collective-permute-start(f32[40,128]{1,0:T(8,128)S(1)} %add_add_fusion.refs_1_), channel_id=1, source_target_pairs={{0,24},{8,16},{16,8},{24,0},{1,25},{9,17},{17,9},{25,1},{2,26},{10... | collective-permute-start | bytes 61448 | tf_op jit(solution)/shard_map/ppermute | solution.py:40
  102.2 4.8 %collective-permute-start.49 = (f32[40,128]{1,0:T(8,128)S(1)}, f32[40,128]{1,0:T(8,128)S(1)}, u32[]{:S(2)}, u32[]{:S(2)}) collective-permute-start(f32[40,128]{1,0:T(8,128)S(1)} %add_add_fusion.refs_1_), channel_id=1, source_target_pairs={{0,16},{8,24},{16,0},{24,8},{1,17},{9,25},{17,1},{25,9},{2,18},{10... | collective-permute-start | bytes 61448 | tf_op jit(solution)/shard_map/ppermute | solution.py:40
  103.1 4.0 %collective-permute-start.50 = (f32[40,128]{1,0:T(8,128)S(1)}, f32[40,128]{1,0:T(8,128)S(1)}, u32[]{:S(2)}, u32[]{:S(2)}) collective-permute-start(f32[40,128]{1,0:T(8,128)S(1)} %add_add_fusion.refs_1_), channel_id=1, source_target_pairs={{0,8},{8,0},{16,24},{24,16},{1,9},{9,1},{17,25},{25,17},{2,10},{10... | collective-permute-start | bytes 61448 | tf_op jit(solution)/shard_map/ppermute | solution.py:40
  (9 other events, 48.9 us)

commit v19 on v17

--- a/solution.py
+++ b/solution.py
@@ -73,12 +73,18 @@
 
 def table_kernel(group, meta, rows_ref, cols_ref, table):
     rows, cols = rows_ref[...], cols_ref[...]
-    apart = lax.div(rows, group) ^ meta[1]
-    halves = lax.rem(apart, 2) * meta[2] + lax.div(apart, 2)
+    apart = lax.div(rows, group) ^ meta[1:2, :]
+    halves = lax.rem(apart, 2) * meta[2:3, :] + lax.div(apart, 2)
     inside = lax.rem(rows, group)
-    table[0:1, :] = (lax.div(cols, group) ^ meta[0]) * group + lax.rem(cols, group)
+    table[0:1, :] = (lax.div(cols, group) ^ meta[0:1, :]) * group + lax.rem(cols, group)
     table[1:2, :] = apart * group + inside
     table[2:3, :] = halves * group + inside
+
+
+def fetch(source, table, arrived):
+    copy = pltpu.make_async_copy(source, table, arrived)
+    copy.start()
+    return copy
 
 
 def fill_ones(panel, vectors_n):
@@ -98,11 +104,14 @@
         ref[...] = jnp.zeros_like(ref)
 
 
-def column_kernel(runs, table, tiles_ref, *refs):
-    parts, (_, own_ref, total, *send_refs, panel) = refs[: len(runs)], refs[len(runs) :]
+def column_kernel(runs, source, tiles_ref, *refs):
+    parts, refs = refs[: len(runs)], refs[len(runs) :]
+    _, own_ref, total, *send_refs, panel, table, arrived = refs
+    copy = fetch(source, table, arrived)
     group, vectors_n, _ = parts[0].shape
     fill(panel, parts, runs)
     fill_ones(panel, vectors_n)
+    copy.wait()
     for t in range(tiles_ref.shape[0]):
         total[table[0, t]] += lax.dot_general(
             panel[table[1, t]], tiles_ref[t], NN, preferred_element_type=F32
@@ -112,12 +121,15 @@
         round_sums(send, total, d * group, group, vectors_n)
 
 
-def row_kernel(runs, table, tiles_ref, *refs):
-    parts, (_, total, swap_ref, panel) = refs[: len(runs)], refs[len(runs) :]
+def row_kernel(runs, source, tiles_ref, *refs):
+    parts, refs = refs[: len(runs)], refs[len(runs) :]
+    _, total, swap_ref, panel, table, arrived = refs
+    copy = fetch(source, table, arrived)
     group, vectors_n, _ = parts[0].shape
     half = swap_ref.shape[0]
     fill(panel, parts, runs)
     fill_ones(panel, vectors_n)
+    copy.wait()
     for t in range(tiles_ref.shape[0]):
         total[table[2, t]] += lax.dot_general(
             panel[table[0, t]], tiles_ref[t], NT, preferred_element_type=F32
@@ -145,25 +157,26 @@
     def panel(count):
         return pltpu.VMEM((count * group, height, width), BF16)
 
+    fetched = [pltpu.SMEM(table.shape, table.dtype), pltpu.SemaphoreType.DMA(())]
     col_own, _, *col_send = call(
         functools.partial(column_kernel, runs[1]),
         [jax.ShapeDtypeStruct((group, height, width), F32), zeros[1]] + [send_shape] * (rows_n - 1),
-        [panel(2 * half)],
+        [panel(2 * half), *fetched],
         24,
         [table, tiles, *row_parts, zeros[1]],
         flops,
-        1,
+        0,
         (),
         {2 + len(row_parts): 1},
     )
     kept, swap = call(
         functools.partial(row_kernel, runs[0]),
         [zeros[0], jax.ShapeDtypeStruct((half, rows, width), BF16)],
-        [panel(rows_n)],
+        [panel(rows_n), *fetched],
         24,
         [table, tiles, *col_parts, zeros[0]],
         flops,
-        1,
+        0,
         [col_own],
         {3 + len(col_parts): 0},
     )
@@ -256,20 +269,24 @@
     )
 
 
-def half_form_kernel(runs, table, tiles_ref, *refs):
-    parts, (out_ref, panel) = refs[:-2], refs[-2:]
+def half_form_kernel(runs, source, tiles_ref, *refs):
+    parts, (out_ref, panel, table, arrived) = refs[:-4], refs[-4:]
+    copy = fetch(source, table, arrived)
     width = panel.shape[2]
     fill(panel, parts, runs)
+    copy.wait()
     for t in range(tiles_ref.shape[0]):
         out_ref[:, t * width : (t + 1) * width] = lax.dot_general(
             panel[table[1, t]], tiles_ref[t], NN, preferred_element_type=F32
         ).astype(BF16)
 
 
-def form_kernel(runs, table, left, gram_ref, *refs):
-    parts, (out_ref, panel, right) = refs[:-3], refs[-3:]
+def form_kernel(runs, source, left, gram_ref, *refs):
+    parts, (out_ref, panel, right, table, arrived) = refs[:-5], refs[-5:]
+    copy = fetch(source, table, arrived)
     _, vectors_n, width = panel.shape
     fill(panel, parts, runs)
+    copy.wait()
     for t in range(right.shape[1] // width):
         right[:, t * width : (t + 1) * width] = panel[table[0, t]]
     form = lax.dot_general(left[...], right[...], NT, preferred_element_type=F32)
@@ -420,13 +437,13 @@
 
     rounded = call(round_kernel, rounded_shape, [], 16, [start])
     meta = jnp.stack([lax.axis_index("row"), lax.axis_index("col"), chips_n]).astype(jnp.int32)
+    meta = jnp.broadcast_to(meta[:, None], (3, tiles.shape[0]))
     table = call(
         functools.partial(table_kernel, group),
         jax.ShapeDtypeStruct((3, tiles.shape[0]), jnp.int32),
         [],
         16,
         [meta, tile_rows[None], tile_cols[None]],
-        smem=1,
     )
     first, rounded, degree = call(
         functools.partial(first_kernel, chips_n),
@@ -451,23 +468,22 @@
         24 * vectors_n * vectors_n * own_nodes,
     )
     col_parts, row_parts = gather(rounded, (gram,))
+    fetched = [pltpu.SMEM(table.shape, table.dtype), pltpu.SemaphoreType.DMA(())]
     left = call(
         functools.partial(half_form_kernel, runs[1]),
         jax.ShapeDtypeStruct(spread, BF16),
-        [pltpu.VMEM((cols_n * group, vectors_n, width), BF16)],
+        [pltpu.VMEM((cols_n * group, vectors_n, width), BF16), *fetched],
         24,
         [table, tiles, *row_parts],
         2 * tiles.size * vectors_n,
-        1,
     )
     sums = call(
         functools.partial(form_kernel, runs[0]),
         jax.ShapeDtypeStruct((vectors_n // 2 + 8, 2 * vectors_n), F32),
-        [pltpu.VMEM((rows_n * group, vectors_n, width), BF16), pltpu.VMEM(spread, BF16)],
+        [pltpu.VMEM((rows_n * group, vectors_n, width), BF16), pltpu.VMEM(spread, BF16), *fetched],
         24,
         [table, left, gram, *col_parts],
         2 * vectors_n * spread[0] * spread[1],
-        1,
     )
     sums = sums + trade(sums, "col", 1)
     sums = tree_sum([*exchange([sums] * (chips_n - 1), "col", 2)[::-1], sums])

time: 99.7 us -> 99.7 us (level)
  no operation moved by 1% of the time
where the time goes in v19:
time: 99.7 us; the launch traced here: 99.5 us
  starting transfers between devices  53.8 us (54%)
  waiting for transfers between devices  28.2 us (28%)
  Pallas kernels  12.8 us (13%)
  local copies, waits for them, and re-layouts  3.64 us (4%)
    ppermute x51, starting transfers between devices, trade(): return lax.ppermute(part, axis, [(i, i ^ d) for i in range(n)])  53.8 us
    ppermute x51, waiting for transfers between devices, trade(): return lax.ppermute(part, axis, [(i, i ^ d) for i in range(n)])  28.2 us
    pallas_call x16, Pallas kernels, call(): pl.pallas_call(lambda *refs: kernel(*refs[len(after):]), out_shape=jax.tr...  12.8 us
    unnamed x12, local copies, waits for them, and re-layouts  3.54 us
  transfers between devices with their start and end apart: 51, of which 30 were waited for; matrix products, arithmetic and copies ran while one was open for 0% of the time, Pallas kernels for 5%

profile of v19, /device:TPU:0, one launch (start us, length us, event | category | flops | bytes accessed | tf_op | source)
XLA Modules:
  0.0 99.5 jit_solution(6818050894850194799)
XLA Ops:
  0.6 0.9 copy-done.2
  1.6 4.1 %collective-permute-start.8 = (bf16[8,64,128]{2,1,0:T(8,128)(2,1)S(1)}, bf16[8,64,128]{2,1,0:T(8,128)(2,1)S(1)}, u32[]{:S(2)}, u32[]{:S(2)}) collective-permute-start(bf16[8,64,128]{2,1,0:T(8,128)(2,1)S(1)} %shard_map.60.refs_2_.refs_3_), channel_id=1, source_target_pairs={{0,16},{8,24},{16,0},{24,8},{1,17},{9,25},{17,1},{25,9},{2,18},{10... | collective-permute-start | bytes 393224 | tf_op jit(solution)/shard_map/ppermute | solution.py:39
  5.7 1.6 %collective-permute-start.7 = (bf16[7,64,128]{2,1,0:T(8,128)(2,1)S(1)}, bf16[7,64,128]{2,1,0:T(8,128)(2,1)S(1)}, u32[]{:S(2)}, u32[]{:S(2)}) collective-permute-start(bf16[7,64,128]{2,1,0:T(8,128)(2,1)S(1)} %slice.24), channel_id=1, source_target_pairs={{0,8},{8,0},{16,24},{24,16},{1,9},{9,1},{17,25},{25,17},{2,10},{10... | collective-permute-start | bytes 344072 | tf_op jit(solution)/shard_map/ppermute | solution.py:39
  7.4 2.4 %collective-permute-start = (bf16[8,64,128]{2,1,0:T(8,128)(2,1)S(1)}, bf16[8,64,128]{2,1,0:T(8,128)(2,1)S(1)}, u32[]{:S(2)}, u32[]{:S(2)}) collective-permute-start(bf16[8,64,128]{2,1,0:T(8,128)(2,1)S(1)} %shard_map.60.refs_2_.refs_3_), channel_id=1, source_target_pairs={{0,6},{1,7},{2,4},{3,5},{4,2},{5,3},{6,0},{7,1},{8,14},{9,15},{10,... | collective-permute-start | bytes 393224 | tf_op jit(solution)/shard_map/ppermute | solution.py:39
  12.6 0.9 collective-permute-start.9
  14.0 1.7 %collective-permute-done.1.refs_4_ = bf16[8,64,128]{2,1,0:T(8,128)(2,1)S(1)} collective-permute-done((bf16[8,64,128]{2,1,0:T(8,128)(2,1)S(1)}, bf16[8,64,128]{2,1,0:T(8,128)(2,1)S(1)}, u32[]{:S(2)}, u32[]{:S(2)}) %collective-permute-start.1) | collective-permute-done | bytes 131104 | tf_op jit(solution)/shard_map/ppermute | solution.py:39
  16.3 0.8 collective-permute-done.5.refs_8_
  17.3 1.2 %copy-done = bf16[1,1,32,128,128]{4,3,2,1,0:T(8,128)(2,1)S(1)} copy-done((bf16[1,1,32,128,128]{4,3,2,1,0:T(8,128)(2,1)S(1)}, bf16[1,1,32,128,128]{4,3,2,1,0:T(8,128)(2,1)}, u32[]{:S(2)}) %copy-start) | copy-done | bytes 1048600
  18.5 1.2 %shard_map.62 = (f32[8,80,128]{2,1,0:T(8,128)S(1)}, f32[32,80,128]{2,1,0:T(8,128)S(1)}, bf16[528,128]{1,0:T(8,128)(2,1)S(1)}, bf16[528,128]{1,0:T(8,128)(2,1)S(1)}, bf16[528,128]{1,0:T(8,128)(2,1)S(1)}) custom-call(s32[3,32]{1,0:T(4,128)S(1)} %shard_map.59.refs_0_.refs_1_, bf16[32,128,128]{2,1,0:T(8,128)(2,1)S(1)} %bitcast.5, ...), custom_call_target="tpu_custom_call", output_to_operand_aliasing={{1}: (10, {})} | custom-call | flops 67108864 | bytes 3408256 | tf_op jit(solution)/shard_map/pallas_call | solution.py:25
  19.7 1.5 %shard_map.63 = (f32[64,80,128]{2,1,0:T(8,128)S(1)}, bf16[4,528,128]{2,1,0:T(8,128)(2,1)S(1)}) custom-call(f32[8,80,128]{2,1,0:T(8,128)S(1)} %get-tuple-element.39.refs_0_.refs_3_, s32[3,32]{1,0:T(4,128)S(1)} %shard_map.59.refs_0_.refs_1_, bf16[32,128,128]{2,1,0:T(8,128)(2,1)S(1)} %bitcast.6, ...), custom_call_target="tpu_custom_call", output_to_operand_aliasing={{0}: (7, {})} | custom-call | flops 67108864 | bytes 4194688 | tf_op jit(solution)/shard_map/pallas_call | solution.py:25
  22.1 1.5 %collective-permute-start.15 = (bf16[528,128]{1,0:T(8,128)(2,1)S(1)}, bf16[528,128]{1,0:T(8,128)(2,1)S(1)}, u32[]{:S(2)}, u32[]{:S(2)}) collective-permute-start(bf16[528,128]{1,0:T(8,128)(2,1)S(1)} %get-tuple-element.51), channel_id=1, source_target_pairs={{0,16},{8,24},{16,0},{24,8},{1,17},{9,25},{17,1},{25,9},{2,18},{10... | collective-permute-start | bytes 405512 | tf_op jit(solution)/shard_map/ppermute | solution.py:39
  23.6 2.4 %collective-permute-start.16 = (bf16[528,128]{1,0:T(8,128)(2,1)S(1)}, bf16[528,128]{1,0:T(8,128)(2,1)S(1)}, u32[]{:S(2)}, u32[]{:S(2)}) collective-permute-start(bf16[528,128]{1,0:T(8,128)(2,1)S(1)} %get-tuple-element.52), channel_id=1, source_target_pairs={{0,24},{8,16},{16,8},{24,0},{1,25},{9,17},{17,9},{25,1},{2,26},{10... | collective-permute-start | bytes 405512 | tf_op jit(solution)/shard_map/ppermute | solution.py:39
  26.1 1.8 %collective-permute-start.11 = (bf16[528,128]{1,0:T(8,128)(2,1)S(1)}, bf16[528,128]{1,0:T(8,128)(2,1)S(1)}, u32[]{:S(2)}, u32[]{:S(2)}) collective-permute-start(bf16[528,128]{1,0:T(8,128)(2,1)S(1)} %get-tuple-element.47), channel_id=1, source_target_pairs={{0,6},{1,7},{2,4},{3,5},{4,2},{5,3},{6,0},{7,1},{8,14},{9,15},{10,... | collective-permute-start | bytes 405512 | tf_op jit(solution)/shard_map/ppermute | solution.py:39
  28.0 1.2 %collective-permute-start.12 = (bf16[528,128]{1,0:T(8,128)(2,1)S(1)}, bf16[528,128]{1,0:T(8,128)(2,1)S(1)}, u32[]{:S(2)}, u32[]{:S(2)}) collective-permute-start(bf16[528,128]{1,0:T(8,128)(2,1)S(1)} %get-tuple-element.48), channel_id=1, source_target_pairs={{0,4},{1,5},{2,6},{3,7},{4,0},{5,1},{6,2},{7,3},{8,12},{9,13},{10,... | collective-permute-start | bytes 405512 | tf_op jit(solution)/shard_map/ppermute | solution.py:39
  29.4 1.5 %collective-permute-start.13 = (bf16[528,128]{1,0:T(8,128)(2,1)S(1)}, bf16[528,128]{1,0:T(8,128)(2,1)S(1)}, u32[]{:S(2)}, u32[]{:S(2)}) collective-permute-start(bf16[528,128]{1,0:T(8,128)(2,1)S(1)} %get-tuple-element.49), channel_id=1, source_target_pairs={{0,2},{1,3},{2,0},{3,1},{4,6},{5,7},{6,4},{7,5},{8,10},{9,11},{10,... | collective-permute-start | bytes 405512 | tf_op jit(solution)/shard_map/ppermute | solution.py:39
  30.9 4.4 %collective-permute-done.15.refs_8_ = bf16[528,128]{1,0:T(8,128)(2,1)S(1)} collective-permute-done((bf16[528,128]{1,0:T(8,128)(2,1)S(1)}, bf16[528,128]{1,0:T(8,128)(2,1)S(1)}, u32[]{:S(2)}, u32[]{:S(2)}) %collective-permute-start.15) | collective-permute-done | bytes 135200 | tf_op jit(solution)/shard_map/ppermute | solution.py:39
  35.5 3.0 %collective-permute-start.25 = (bf16[8,64,128]{2,1,0:T(8,128)(2,1)S(1)}, bf16[8,64,128]{2,1,0:T(8,128)(2,1)S(1)}, u32[]{:S(2)}, u32[]{:S(2)}) collective-permute-start(bf16[8,64,128]{2,1,0:T(8,128)(2,1)S(1)} %get-tuple-element.55.refs_2_.refs_3_), channel_id=1, source_target_pairs={{0,16},{8,24},{16,0},{24,8},{1,17},{9,25},{17,1},{25,9},{2,18},{10... | collective-permute-start | bytes 393224 | tf_op jit(solution)/shard_map/ppermute | solution.py:39
  38.6 2.5 %collective-permute-start.17 = (bf16[8,64,128]{2,1,0:T(8,128)(2,1)S(1)}, bf16[8,64,128]{2,1,0:T(8,128)(2,1)S(1)}, u32[]{:S(2)}, u32[]{:S(2)}) collective-permute-start(bf16[8,64,128]{2,1,0:T(8,128)(2,1)S(1)} %get-tuple-element.55.refs_2_.refs_3_), channel_id=1, source_target_pairs={{0,6},{1,7},{2,4},{3,5},{4,2},{5,3},{6,0},{7,1},{8,14},{9,15},{10,... | collective-permute-start | bytes 393224 | tf_op jit(solution)/shard_map/ppermute | solution.py:39
  42.3 1.7 %collective-permute-done.24.refs_5_ = bf16[7,64,128]{2,1,0:T(8,128)(2,1)S(1)} collective-permute-done((bf16[7,64,128]{2,1,0:T(8,128)(2,1)S(1)}, bf16[7,64,128]{2,1,0:T(8,128)(2,1)S(1)}, u32[]{:S(2)}, u32[]{:S(2)}) %collective-permute-start.24) | collective-permute-done | bytes 114720 | tf_op jit(solution)/shard_map/ppermute | solution.py:39
  44.2 1.3 %collective-permute-start.26 = (bf16[9,64,128]{2,1,0:T(8,128)(2,1)S(1)}, bf16[9,64,128]{2,1,0:T(8,128)(2,1)S(1)}, u32[]{:S(2)}, u32[]{:S(2)}) collective-permute-start(bf16[9,64,128]{2,1,0:T(8,128)(2,1)S(1)} %pad_maximum_fusion.1), channel_id=1, source_target_pairs={{0,8},{8,0},{16,24},{24,16},{1,9},{9,1},{17,25},{25,17},{2,10},{10... | collective-permute-start | bytes 442376 | tf_op jit(solution)/shard_map/ppermute | solution.py:39
  47.1 0.8 collective-permute-done.22.refs_8_
  48.1 1.0 %shard_map.67 = (f32[8,64,128]{2,1,0:T(8,128)S(1)}, f32[32,64,128]{2,1,0:T(8,128)S(1)}, bf16[512,128]{1,0:T(8,128)(2,1)S(1)}, bf16[512,128]{1,0:T(8,128)(2,1)S(1)}, bf16[512,128]{1,0:T(8,128)(2,1)S(1)}) custom-call(s32[3,32]{1,0:T(4,128)S(1)} %shard_map.59.refs_0_.refs_1_, bf16[32,128,128]{2,1,0:T(8,128)(2,1)S(1)} %bitcast.7, ...), custom_call_target="tpu_custom_call", output_to_operand_aliasing={{1}: (10, {})} | custom-call | flops 67108864 | bytes 3146112 | tf_op jit(solution)/shard_map/pallas_call | solution.py:25
  49.4 1.4 %shard_map.68 = (f32[64,64,128]{2,1,0:T(8,128)S(1)}, bf16[4,512,128]{2,1,0:T(8,128)(2,1)S(1)}) custom-call(f32[8,64,128]{2,1,0:T(8,128)S(1)} %get-tuple-element.57.refs_0_.refs_4_, s32[3,32]{1,0:T(4,128)S(1)} %shard_map.59.refs_0_.refs_1_, bf16[32,128,128]{2,1,0:T(8,128)(2,1)S(1)} %bitcast.8, ...), custom_call_target="tpu_custom_call", output_to_operand_aliasing={{0}: (7, {})} | custom-call | flops 67108864 | bytes 3670400 | tf_op jit(solution)/shard_map/pallas_call | solution.py:25
  51.0 2.0 %collective-permute-start.31 = (bf16[512,128]{1,0:T(8,128)(2,1)S(1)}, bf16[512,128]{1,0:T(8,128)(2,1)S(1)}, u32[]{:S(2)}, u32[]{:S(2)}) collective-permute-start(bf16[512,128]{1,0:T(8,128)(2,1)S(1)} %get-tuple-element.67), channel_id=1, source_target_pairs={{0,8},{8,0},{16,24},{24,16},{1,9},{9,1},{17,25},{25,17},{2,10},{10... | collective-permute-start | bytes 393224 | tf_op jit(solution)/shard_map/ppermute | solution.py:39
  53.5 1.9 %collective-permute-start.33 = (bf16[512,128]{1,0:T(8,128)(2,1)S(1)}, bf16[512,128]{1,0:T(8,128)(2,1)S(1)}, u32[]{:S(2)}, u32[]{:S(2)}) collective-permute-start(bf16[512,128]{1,0:T(8,128)(2,1)S(1)} %get-tuple-element.69), channel_id=1, source_target_pairs={{0,24},{8,16},{16,8},{24,0},{1,25},{9,17},{17,9},{25,1},{2,26},{10... | collective-permute-start | bytes 393224 | tf_op jit(solution)/shard_map/ppermute | solution.py:39
  55.5 2.7 %collective-permute-start.28 = (bf16[512,128]{1,0:T(8,128)(2,1)S(1)}, bf16[512,128]{1,0:T(8,128)(2,1)S(1)}, u32[]{:S(2)}, u32[]{:S(2)}) collective-permute-start(bf16[512,128]{1,0:T(8,128)(2,1)S(1)} %get-tuple-element.64), channel_id=1, source_target_pairs={{0,6},{1,7},{2,4},{3,5},{4,2},{5,3},{6,0},{7,1},{8,14},{9,15},{10,... | collective-permute-start | bytes 393224 | tf_op jit(solution)/shard_map/ppermute | solution.py:39
  58.5 1.7 %collective-permute-start.30 = (bf16[512,128]{1,0:T(8,128)(2,1)S(1)}, bf16[512,128]{1,0:T(8,128)(2,1)S(1)}, u32[]{:S(2)}, u32[]{:S(2)}) collective-permute-start(bf16[512,128]{1,0:T(8,128)(2,1)S(1)} %get-tuple-element.66), channel_id=1, source_target_pairs={{0,2},{1,3},{2,0},{3,1},{4,6},{5,7},{6,4},{7,5},{8,10},{9,11},{10,... | collective-permute-start | bytes 393224 | tf_op jit(solution)/shard_map/ppermute | solution.py:39
  60.2 5.7 %collective-permute-done.32.refs_9_ = bf16[512,128]{1,0:T(8,128)(2,1)S(1)} collective-permute-done((bf16[512,128]{1,0:T(8,128)(2,1)S(1)}, bf16[512,128]{1,0:T(8,128)(2,1)S(1)}, u32[]{:S(2)}, u32[]{:S(2)}) %collective-permute-start.32) | collective-permute-done | bytes 131104 | tf_op jit(solution)/shard_map/ppermute | solution.py:39
  66.1 2.5 %collective-permute-start.42 = (bf16[8,64,128]{2,1,0:T(8,128)(2,1)S(1)}, bf16[8,64,128]{2,1,0:T(8,128)(2,1)S(1)}, u32[]{:S(2)}, u32[]{:S(2)}) collective-permute-start(bf16[8,64,128]{2,1,0:T(8,128)(2,1)S(1)} %get-tuple-element.71.refs_2_.refs_3_), channel_id=1, source_target_pairs={{0,16},{8,24},{16,0},{24,8},{1,17},{9,25},{17,1},{25,9},{2,18},{10... | collective-permute-start | bytes 393224 | tf_op jit(solution)/shard_map/ppermute | solution.py:39
  68.8 1.9 %collective-permute-start.34 = (bf16[8,64,128]{2,1,0:T(8,128)(2,1)S(1)}, bf16[8,64,128]{2,1,0:T(8,128)(2,1)S(1)}, u32[]{:S(2)}, u32[]{:S(2)}) collective-permute-start(bf16[8,64,128]{2,1,0:T(8,128)(2,1)S(1)} %get-tuple-element.71.refs_2_.refs_3_), channel_id=1, source_target_pairs={{0,6},{1,7},{2,4},{3,5},{4,2},{5,3},{6,0},{7,1},{8,14},{9,15},{10,... | collective-permute-start | bytes 393224 | tf_op jit(solution)/shard_map/ppermute | solution.py:39
  70.6 1.1 %collective-permute-start.35 = (bf16[8,64,128]{2,1,0:T(8,128)(2,1)S(1)}, bf16[8,64,128]{2,1,0:T(8,128)(2,1)S(1)}, u32[]{:S(2)}, u32[]{:S(2)}) collective-permute-start(bf16[8,64,128]{2,1,0:T(8,128)(2,1)S(1)} %get-tuple-element.71.refs_2_.refs_3_), channel_id=1, source_target_pairs={{0,4},{1,5},{2,6},{3,7},{4,0},{5,1},{6,2},{7,3},{8,12},{9,13},{10,... | collective-permute-start | bytes 393224 | tf_op jit(solution)/shard_map/ppermute | solution.py:39
  73.0 1.5 %collective-permute-done.41.refs_5_ = bf16[7,64,128]{2,1,0:T(8,128)(2,1)S(1)} collective-permute-done((bf16[7,64,128]{2,1,0:T(8,128)(2,1)S(1)}, bf16[7,64,128]{2,1,0:T(8,128)(2,1)S(1)}, u32[]{:S(2)}, u32[]{:S(2)}) %collective-permute-start.41) | collective-permute-done | bytes 114720 | tf_op jit(solution)/shard_map/ppermute | solution.py:39
  74.8 1.0 collective-permute-start.43
  77.4 0.7 collective-permute-done.39.refs_8_
  78.3 1.0 shard_map.71.refs_1_
  80.0 1.2 %shard_map.73 = f32[40,128]{1,0:T(8,128)S(1)} custom-call(s32[3,32]{1,0:T(4,128)S(1)} %shard_map.59.refs_0_.refs_1_, bf16[64,4096]{1,0:T(8,128)(2,1)S(1)} %shard_map.71.refs_1_, f32[64,128]{1,0:T(8,128)S(1)} %shard_map.72.refs_2_, bf16[8,64,128]{2,1,0:T(8,128)(2,1)S(1)} %get-tuple-element.71.refs_2_.refs_3_, ...), custom_call_target="tpu_custom_call" | custom-call | flops 33554432 | bytes 1081728 | tf_op jit(solution)/shard_map/pallas_call | solution.py:25
  81.3 1.2 %collective-permute-done.44 = f32[40,128]{1,0:T(8,128)S(1)} collective-permute-done((f32[40,128]{1,0:T(8,128)S(1)}, f32[40,128]{1,0:T(8,128)S(1)}, u32[]{:S(2)}, u32[]{:S(2)}) %collective-permute-start.44) | collective-permute-done | bytes 20512 | tf_op jit(solution)/shard_map/ppermute | solution.py:39
  82.4 1.1 %collective-permute-start.45 = (f32[40,128]{1,0:T(8,128)S(1)}, f32[40,128]{1,0:T(8,128)S(1)}, u32[]{:S(2)}, u32[]{:S(2)}) collective-permute-start(f32[40,128]{1,0:T(8,128)S(1)} %add.12), channel_id=1, source_target_pairs={{0,6},{1,7},{2,4},{3,5},{4,2},{5,3},{6,0},{7,1},{8,14},{9,15},{10,... | collective-permute-start | bytes 61448 | tf_op jit(solution)/shard_map/ppermute | solution.py:39
  83.6 1.5 %collective-permute-start.46 = (f32[40,128]{1,0:T(8,128)S(1)}, f32[40,128]{1,0:T(8,128)S(1)}, u32[]{:S(2)}, u32[]{:S(2)}) collective-permute-start(f32[40,128]{1,0:T(8,128)S(1)} %add.12), channel_id=1, source_target_pairs={{0,4},{1,5},{2,6},{3,7},{4,0},{5,1},{6,2},{7,3},{8,12},{9,13},{10,... | collective-permute-start | bytes 61448 | tf_op jit(solution)/shard_map/ppermute | solution.py:39
  85.1 0.9 collective-permute-start.47
  85.9 1.2 %collective-permute-done.45 = f32[40,128]{1,0:T(8,128)S(1)} collective-permute-done((f32[40,128]{1,0:T(8,128)S(1)}, f32[40,128]{1,0:T(8,128)S(1)}, u32[]{:S(2)}, u32[]{:S(2)}) %collective-permute-start.45) | collective-permute-done | bytes 20512 | tf_op jit(solution)/shard_map/ppermute | solution.py:39
  87.3 1.5 %collective-permute-done.47 = f32[40,128]{1,0:T(8,128)S(1)} collective-permute-done((f32[40,128]{1,0:T(8,128)S(1)}, f32[40,128]{1,0:T(8,128)S(1)}, u32[]{:S(2)}, u32[]{:S(2)}) %collective-permute-start.47) | collective-permute-done | bytes 20512 | tf_op jit(solution)/shard_map/ppermute | solution.py:39
  88.8 2.0 %collective-permute-start.48 = (f32[40,128]{1,0:T(8,128)S(1)}, f32[40,128]{1,0:T(8,128)S(1)}, u32[]{:S(2)}, u32[]{:S(2)}) collective-permute-start(f32[40,128]{1,0:T(8,128)S(1)} %add_add_fusion.refs_1_), channel_id=1, source_target_pairs={{0,24},{8,16},{16,8},{24,0},{1,25},{9,17},{17,9},{25,1},{2,26},{10... | collective-permute-start | bytes 61448 | tf_op jit(solution)/shard_map/ppermute | solution.py:39
  90.9 0.7 collective-permute-start.49
  91.6 1.7 %collective-permute-start.50 = (f32[40,128]{1,0:T(8,128)S(1)}, f32[40,128]{1,0:T(8,128)S(1)}, u32[]{:S(2)}, u32[]{:S(2)}) collective-permute-start(f32[40,128]{1,0:T(8,128)S(1)} %add_add_fusion.refs_1_), channel_id=1, source_target_pairs={{0,8},{8,0},{16,24},{24,16},{1,9},{9,1},{17,25},{25,17},{2,10},{10... | collective-permute-start | bytes 61448 | tf_op jit(solution)/shard_map/ppermute | solution.py:39
  93.3 1.2 %collective-permute-done.48.refs_2_ = f32[40,128]{1,0:T(8,128)S(1)} collective-permute-done((f32[40,128]{1,0:T(8,128)S(1)}, f32[40,128]{1,0:T(8,128)S(1)}, u32[]{:S(2)}, u32[]{:S(2)}) %collective-permute-start.48) | collective-permute-done | bytes 20512 | tf_op jit(solution)/shard_map/ppermute | solution.py:39
  94.5 1.2 %collective-permute-done.49.refs_3_ = f32[40,128]{1,0:T(8,128)S(1)} collective-permute-done((f32[40,128]{1,0:T(8,128)S(1)}, f32[40,128]{1,0:T(8,128)S(1)}, u32[]{:S(2)}, u32[]{:S(2)}) %collective-permute-start.49) | collective-permute-done | bytes 20512 | tf_op jit(solution)/shard_map/ppermute | solution.py:39
  95.7 3.8 %shard_map.74 = (f32[64,1024]{1,0:T(8,128)}, f32[64,64]{1,0:T(8,128)}) custom-call(f32[64,1024]{1,0:T(8,128)S(1)} %get-tuple-element.70.refs_0_, f32[40,128]{1,0:T(8,128)S(1)} %add_add_fusion.refs_1_, f32[40,128]{1,0:T(8,128)S(1)} %collective-permute-done.48.refs_2_, f32[40,128]{1,0:T(8,128)S(1)} %collective-permute-done.49.refs_3_, ...), custom_call_target="tpu_custom_call" | custom-call | bytes 344064 | tf_op jit(solution)/shard_map/pallas_call | solution.py:25
  (95 shorter events, 14.8 us)
Async XLA Ops:
  1.6 11.0 %collective-permute-start.8 = (bf16[8,64,128]{2,1,0:T(8,128)(2,1)S(1)}, bf16[8,64,128]{2,1,0:T(8,128)(2,1)S(1)}, u32[]{:S(2)}, u32[]{:S(2)}) collective-permute-start(bf16[8,64,128]{2,1,0:T(8,128)(2,1)S(1)} %shard_map.60.refs_2_.refs_3_), channel_id=1, source_target_pairs={{0,16},{8,24},{16,0},{24,8},{1,17},{9,25},{17,1},{25,9},{2,18},{10... | collective-permute-start | bytes 393224 | tf_op jit(solution)/shard_map/ppermute | solution.py:39
  5.7 6.9 %collective-permute-start.7 = (bf16[7,64,128]{2,1,0:T(8,128)(2,1)S(1)}, bf16[7,64,128]{2,1,0:T(8,128)(2,1)S(1)}, u32[]{:S(2)}, u32[]{:S(2)}) collective-permute-start(bf16[7,64,128]{2,1,0:T(8,128)(2,1)S(1)} %slice.24), channel_id=1, source_target_pairs={{0,8},{8,0},{16,24},{24,16},{1,9},{9,1},{17,25},{25,17},{2,10},{10... | collective-permute-start | bytes 344072 | tf_op jit(solution)/shard_map/ppermute | solution.py:39
  7.4 6.6 %collective-permute-start = (bf16[8,64,128]{2,1,0:T(8,128)(2,1)S(1)}, bf16[8,64,128]{2,1,0:T(8,128)(2,1)S(1)}, u32[]{:S(2)}, u32[]{:S(2)}) collective-permute-start(bf16[8,64,128]{2,1,0:T(8,128)(2,1)S(1)} %shard_map.60.refs_2_.refs_3_), channel_id=1, source_target_pairs={{0,6},{1,7},{2,4},{3,5},{4,2},{5,3},{6,0},{7,1},{8,14},{9,15},{10,... | collective-permute-start | bytes 393224 | tf_op jit(solution)/shard_map/ppermute | solution.py:39
  9.8 5.9 %collective-permute-start.1 = (bf16[8,64,128]{2,1,0:T(8,128)(2,1)S(1)}, bf16[8,64,128]{2,1,0:T(8,128)(2,1)S(1)}, u32[]{:S(2)}, u32[]{:S(2)}) collective-permute-start(bf16[8,64,128]{2,1,0:T(8,128)(2,1)S(1)} %shard_map.60.refs_2_.refs_3_), channel_id=1, source_target_pairs={{0,4},{1,5},{2,6},{3,7},{4,0},{5,1},{6,2},{7,3},{8,12},{9,13},{10,... | collective-permute-start | bytes 393224 | tf_op jit(solution)/shard_map/ppermute | solution.py:39
  10.3 5.5 %collective-permute-start.2 = (bf16[8,64,128]{2,1,0:T(8,128)(2,1)S(1)}, bf16[8,64,128]{2,1,0:T(8,128)(2,1)S(1)}, u32[]{:S(2)}, u32[]{:S(2)}) collective-permute-start(bf16[8,64,128]{2,1,0:T(8,128)(2,1)S(1)} %shard_map.60.refs_2_.refs_3_), channel_id=1, source_target_pairs={{0,2},{1,3},{2,0},{3,1},{4,6},{5,7},{6,4},{7,5},{8,10},{9,11},{10,... | collective-permute-start | bytes 393224 | tf_op jit(solution)/shard_map/ppermute | solution.py:39
  12.6 7.0 %collective-permute-start.9 = (bf16[9,64,128]{2,1,0:T(8,128)(2,1)S(1)}, bf16[9,64,128]{2,1,0:T(8,128)(2,1)S(1)}, u32[]{:S(2)}, u32[]{:S(2)}) collective-permute-start(bf16[9,64,128]{2,1,0:T(8,128)(2,1)S(1)} %pad_maximum_fusion), channel_id=1, source_target_pairs={{0,8},{8,0},{16,24},{24,16},{1,9},{9,1},{17,25},{25,17},{2,10},{10... | collective-permute-start | bytes 442376 | tf_op jit(solution)/shard_map/ppermute | solution.py:39
  13.5 2.8 %collective-permute-start.3 = (bf16[8,64,128]{2,1,0:T(8,128)(2,1)S(1)}, bf16[8,64,128]{2,1,0:T(8,128)(2,1)S(1)}, u32[]{:S(2)}, u32[]{:S(2)}) collective-permute-start(bf16[8,64,128]{2,1,0:T(8,128)(2,1)S(1)} %shard_map.60.refs_2_.refs_3_), channel_id=1, source_target_pairs={{0,1},{1,0},{2,3},{3,2},{4,5},{5,4},{6,7},{7,6},{8,9},{9,8},{10,11... | collective-permute-start | bytes 393224 | tf_op jit(solution)/shard_map/ppermute | solution.py:39
  13.9 2.3 %collective-permute-start.4 = (bf16[8,64,128]{2,1,0:T(8,128)(2,1)S(1)}, bf16[8,64,128]{2,1,0:T(8,128)(2,1)S(1)}, u32[]{:S(2)}, u32[]{:S(2)}) collective-permute-start(bf16[8,64,128]{2,1,0:T(8,128)(2,1)S(1)} %collective-permute-done.refs_3_), channel_id=1, source_target_pairs={{0,1},{1,0},{2,3},{3,2},{4,5},{5,4},{6,7},{7,6},{8,9},{9,8},{10,11... | collective-permute-start | bytes 393224 | tf_op jit(solution)/shard_map/ppermute | solution.py:39
  15.7 1.3 %collective-permute-start.5 = (bf16[8,64,128]{2,1,0:T(8,128)(2,1)S(1)}, bf16[8,64,128]{2,1,0:T(8,128)(2,1)S(1)}, u32[]{:S(2)}, u32[]{:S(2)}) collective-permute-start(bf16[8,64,128]{2,1,0:T(8,128)(2,1)S(1)} %collective-permute-done.1.refs_4_), channel_id=1, source_target_pairs={{0,1},{1,0},{2,3},{3,2},{4,5},{5,4},{6,7},{7,6},{8,9},{9,8},{10,11... | collective-permute-start | bytes 393224 | tf_op jit(solution)/shard_map/ppermute | solution.py:39
  15.8 1.4 %collective-permute-start.6 = (bf16[8,64,128]{2,1,0:T(8,128)(2,1)S(1)}, bf16[8,64,128]{2,1,0:T(8,128)(2,1)S(1)}, u32[]{:S(2)}, u32[]{:S(2)}) collective-permute-start(bf16[8,64,128]{2,1,0:T(8,128)(2,1)S(1)} %collective-permute-done.2.refs_5_), channel_id=1, source_target_pairs={{0,1},{1,0},{2,3},{3,2},{4,5},{5,4},{6,7},{7,6},{8,9},{9,8},{10,11... | collective-permute-start | bytes 393224 | tf_op jit(solution)/shard_map/ppermute | solution.py:39
  21.2 4.8 %collective-permute-start.10 = (bf16[4,528,128]{2,1,0:T(8,128)(2,1)S(1)}, bf16[4,528,128]{2,1,0:T(8,128)(2,1)S(1)}, u32[]{:S(2)}, u32[]{:S(2)}) collective-permute-start(bf16[4,528,128]{2,1,0:T(8,128)(2,1)S(1)} %get-tuple-element.44), channel_id=1, source_target_pairs={{0,1},{1,0},{2,3},{3,2},{4,5},{5,4},{6,7},{7,6},{8,9},{9,8},{10,11... | collective-permute-start | bytes 1622024 | tf_op jit(solution)/shard_map/ppermute | solution.py:39
  21.6 7.8 %collective-permute-start.14 = (bf16[528,128]{1,0:T(8,128)(2,1)S(1)}, bf16[528,128]{1,0:T(8,128)(2,1)S(1)}, u32[]{:S(2)}, u32[]{:S(2)}) collective-permute-start(bf16[528,128]{1,0:T(8,128)(2,1)S(1)} %get-tuple-element.50), channel_id=1, source_target_pairs={{0,8},{8,0},{16,24},{24,16},{1,9},{9,1},{17,25},{25,17},{2,10},{10... | collective-permute-start | bytes 405512 | tf_op jit(solution)/shard_map/ppermute | solution.py:39
  22.1 13.2 %collective-permute-start.15 = (bf16[528,128]{1,0:T(8,128)(2,1)S(1)}, bf16[528,128]{1,0:T(8,128)(2,1)S(1)}, u32[]{:S(2)}, u32[]{:S(2)}) collective-permute-start(bf16[528,128]{1,0:T(8,128)(2,1)S(1)} %get-tuple-element.51), channel_id=1, source_target_pairs={{0,16},{8,24},{16,0},{24,8},{1,17},{9,25},{17,1},{25,9},{2,18},{10... | collective-permute-start | bytes 405512 | tf_op jit(solution)/shard_map/ppermute | solution.py:39
  23.6 11.6 %collective-permute-start.16 = (bf16[528,128]{1,0:T(8,128)(2,1)S(1)}, bf16[528,128]{1,0:T(8,128)(2,1)S(1)}, u32[]{:S(2)}, u32[]{:S(2)}) collective-permute-start(bf16[528,128]{1,0:T(8,128)(2,1)S(1)} %get-tuple-element.52), channel_id=1, source_target_pairs={{0,24},{8,16},{16,8},{24,0},{1,25},{9,17},{17,9},{25,1},{2,26},{10... | collective-permute-start | bytes 405512 | tf_op jit(solution)/shard_map/ppermute | solution.py:39
  26.1 9.1 %collective-permute-start.11 = (bf16[528,128]{1,0:T(8,128)(2,1)S(1)}, bf16[528,128]{1,0:T(8,128)(2,1)S(1)}, u32[]{:S(2)}, u32[]{:S(2)}) collective-permute-start(bf16[528,128]{1,0:T(8,128)(2,1)S(1)} %get-tuple-element.47), channel_id=1, source_target_pairs={{0,6},{1,7},{2,4},{3,5},{4,2},{5,3},{6,0},{7,1},{8,14},{9,15},{10,... | collective-permute-start | bytes 405512 | tf_op jit(solution)/shard_map/ppermute | solution.py:39
  28.0 7.3 %collective-permute-start.12 = (bf16[528,128]{1,0:T(8,128)(2,1)S(1)}, bf16[528,128]{1,0:T(8,128)(2,1)S(1)}, u32[]{:S(2)}, u32[]{:S(2)}) collective-permute-start(bf16[528,128]{1,0:T(8,128)(2,1)S(1)} %get-tuple-element.48), channel_id=1, source_target_pairs={{0,4},{1,5},{2,6},{3,7},{4,0},{5,1},{6,2},{7,3},{8,12},{9,13},{10,... | collective-permute-start | bytes 405512 | tf_op jit(solution)/shard_map/ppermute | solution.py:39
  29.4 5.9 %collective-permute-start.13 = (bf16[528,128]{1,0:T(8,128)(2,1)S(1)}, bf16[528,128]{1,0:T(8,128)(2,1)S(1)}, u32[]{:S(2)}, u32[]{:S(2)}) collective-permute-start(bf16[528,128]{1,0:T(8,128)(2,1)S(1)} %get-tuple-element.49), channel_id=1, source_target_pairs={{0,2},{1,3},{2,0},{3,1},{4,6},{5,7},{6,4},{7,5},{8,10},{9,11},{10,... | collective-permute-start | bytes 405512 | tf_op jit(solution)/shard_map/ppermute | solution.py:39
  35.5 8.7 %collective-permute-start.25 = (bf16[8,64,128]{2,1,0:T(8,128)(2,1)S(1)}, bf16[8,64,128]{2,1,0:T(8,128)(2,1)S(1)}, u32[]{:S(2)}, u32[]{:S(2)}) collective-permute-start(bf16[8,64,128]{2,1,0:T(8,128)(2,1)S(1)} %get-tuple-element.55.refs_2_.refs_3_), channel_id=1, source_target_pairs={{0,16},{8,24},{16,0},{24,8},{1,17},{9,25},{17,1},{25,9},{2,18},{10... | collective-permute-start | bytes 393224 | tf_op jit(solution)/shard_map/ppermute | solution.py:39
  38.5 5.5 %collective-permute-start.24 = (bf16[7,64,128]{2,1,0:T(8,128)(2,1)S(1)}, bf16[7,64,128]{2,1,0:T(8,128)(2,1)S(1)}, u32[]{:S(2)}, u32[]{:S(2)}) collective-permute-start(bf16[7,64,128]{2,1,0:T(8,128)(2,1)S(1)} %slice.20), channel_id=1, source_target_pairs={{0,8},{8,0},{16,24},{24,16},{1,9},{9,1},{17,25},{25,17},{2,10},{10... | collective-permute-start | bytes 344072 | tf_op jit(solution)/shard_map/ppermute | solution.py:39
  38.6 7.0 %collective-permute-start.17 = (bf16[8,64,128]{2,1,0:T(8,128)(2,1)S(1)}, bf16[8,64,128]{2,1,0:T(8,128)(2,1)S(1)}, u32[]{:S(2)}, u32[]{:S(2)}) collective-permute-start(bf16[8,64,128]{2,1,0:T(8,128)(2,1)S(1)} %get-tuple-element.55.refs_2_.refs_3_), channel_id=1, source_target_pairs={{0,6},{1,7},{2,4},{3,5},{4,2},{5,3},{6,0},{7,1},{8,14},{9,15},{10,... | collective-permute-start | bytes 393224 | tf_op jit(solution)/shard_map/ppermute | solution.py:39
  41.0 5.5 %collective-permute-start.18 = (bf16[8,64,128]{2,1,0:T(8,128)(2,1)S(1)}, bf16[8,64,128]{2,1,0:T(8,128)(2,1)S(1)}, u32[]{:S(2)}, u32[]{:S(2)}) collective-permute-start(bf16[8,64,128]{2,1,0:T(8,128)(2,1)S(1)} %get-tuple-element.55.refs_2_.refs_3_), channel_id=1, source_target_pairs={{0,4},{1,5},{2,6},{3,7},{4,0},{5,1},{6,2},{7,3},{8,12},{9,13},{10,... | collective-permute-start | bytes 393224 | tf_op jit(solution)/shard_map/ppermute | solution.py:39
  41.6 5.1 %collective-permute-start.19 = (bf16[8,64,128]{2,1,0:T(8,128)(2,1)S(1)}, bf16[8,64,128]{2,1,0:T(8,128)(2,1)S(1)}, u32[]{:S(2)}, u32[]{:S(2)}) collective-permute-start(bf16[8,64,128]{2,1,0:T(8,128)(2,1)S(1)} %get-tuple-element.55.refs_2_.refs_3_), channel_id=1, source_target_pairs={{0,2},{1,3},{2,0},{3,1},{4,6},{5,7},{6,4},{7,5},{8,10},{9,11},{10,... | collective-permute-start | bytes 393224 | tf_op jit(solution)/shard_map/ppermute | solution.py:39
  44.2 5.2 %collective-permute-start.26 = (bf16[9,64,128]{2,1,0:T(8,128)(2,1)S(1)}, bf16[9,64,128]{2,1,0:T(8,128)(2,1)S(1)}, u32[]{:S(2)}, u32[]{:S(2)}) collective-permute-start(bf16[9,64,128]{2,1,0:T(8,128)(2,1)S(1)} %pad_maximum_fusion.1), channel_id=1, source_target_pairs={{0,8},{8,0},{16,24},{24,16},{1,9},{9,1},{17,25},{25,17},{2,10},{10... | collective-permute-start | bytes 442376 | tf_op jit(solution)/shard_map/ppermute | solution.py:39
  45.5 1.6 %collective-permute-start.20 = (bf16[8,64,128]{2,1,0:T(8,128)(2,1)S(1)}, bf16[8,64,128]{2,1,0:T(8,128)(2,1)S(1)}, u32[]{:S(2)}, u32[]{:S(2)}) collective-permute-start(bf16[8,64,128]{2,1,0:T(8,128)(2,1)S(1)} %get-tuple-element.55.refs_2_.refs_3_), channel_id=1, source_target_pairs={{0,1},{1,0},{2,3},{3,2},{4,5},{5,4},{6,7},{7,6},{8,9},{9,8},{10,11... | collective-permute-start | bytes 393224 | tf_op jit(solution)/shard_map/ppermute | solution.py:39
  45.6 1.5 %collective-permute-start.21 = (bf16[8,64,128]{2,1,0:T(8,128)(2,1)S(1)}, bf16[8,64,128]{2,1,0:T(8,128)(2,1)S(1)}, u32[]{:S(2)}, u32[]{:S(2)}) collective-permute-start(bf16[8,64,128]{2,1,0:T(8,128)(2,1)S(1)} %collective-permute-done.17.refs_3_), channel_id=1, source_target_pairs={{0,1},{1,0},{2,3},{3,2},{4,5},{5,4},{6,7},{7,6},{8,9},{9,8},{10,11... | collective-permute-start | bytes 393224 | tf_op jit(solution)/shard_map/ppermute | solution.py:39
  46.5 1.3 %collective-permute-start.22 = (bf16[8,64,128]{2,1,0:T(8,128)(2,1)S(1)}, bf16[8,64,128]{2,1,0:T(8,128)(2,1)S(1)}, u32[]{:S(2)}, u32[]{:S(2)}) collective-permute-start(bf16[8,64,128]{2,1,0:T(8,128)(2,1)S(1)} %collective-permute-done.18.refs_4_), channel_id=1, source_target_pairs={{0,1},{1,0},{2,3},{3,2},{4,5},{5,4},{6,7},{7,6},{8,9},{9,8},{10,11... | collective-permute-start | bytes 393224 | tf_op jit(solution)/shard_map/ppermute | solution.py:39
  46.6 1.4 %collective-permute-start.23 = (bf16[8,64,128]{2,1,0:T(8,128)(2,1)S(1)}, bf16[8,64,128]{2,1,0:T(8,128)(2,1)S(1)}, u32[]{:S(2)}, u32[]{:S(2)}) collective-permute-start(bf16[8,64,128]{2,1,0:T(8,128)(2,1)S(1)} %collective-permute-done.19.refs_5_), channel_id=1, source_target_pairs={{0,1},{1,0},{2,3},{3,2},{4,5},{5,4},{6,7},{7,6},{8,9},{9,8},{10,11... | collective-permute-start | bytes 393224 | tf_op jit(solution)/shard_map/ppermute | solution.py:39
  50.9 4.5 %collective-permute-start.27 = (bf16[4,512,128]{2,1,0:T(8,128)(2,1)S(1)}, bf16[4,512,128]{2,1,0:T(8,128)(2,1)S(1)}, u32[]{:S(2)}, u32[]{:S(2)}) collective-permute-start(bf16[4,512,128]{2,1,0:T(8,128)(2,1)S(1)} %get-tuple-element.62), channel_id=1, source_target_pairs={{0,1},{1,0},{2,3},{3,2},{4,5},{5,4},{6,7},{7,6},{8,9},{9,8},{10,11... | collective-permute-start | bytes 1572872 | tf_op jit(solution)/shard_map/ppermute | solution.py:39
  51.0 7.6 %collective-permute-start.31 = (bf16[512,128]{1,0:T(8,128)(2,1)S(1)}, bf16[512,128]{1,0:T(8,128)(2,1)S(1)}, u32[]{:S(2)}, u32[]{:S(2)}) collective-permute-start(bf16[512,128]{1,0:T(8,128)(2,1)S(1)} %get-tuple-element.67), channel_id=1, source_target_pairs={{0,8},{8,0},{16,24},{24,16},{1,9},{9,1},{17,25},{25,17},{2,10},{10... | collective-permute-start | bytes 393224 | tf_op jit(solution)/shard_map/ppermute | solution.py:39
  53.0 12.9 %collective-permute-start.32 = (bf16[512,128]{1,0:T(8,128)(2,1)S(1)}, bf16[512,128]{1,0:T(8,128)(2,1)S(1)}, u32[]{:S(2)}, u32[]{:S(2)}) collective-permute-start(bf16[512,128]{1,0:T(8,128)(2,1)S(1)} %get-tuple-element.68), channel_id=1, source_target_pairs={{0,16},{8,24},{16,0},{24,8},{1,17},{9,25},{17,1},{25,9},{2,18},{10... | collective-permute-start | bytes 393224 | tf_op jit(solution)/shard_map/ppermute | solution.py:39
  53.5 12.4 %collective-permute-start.33 = (bf16[512,128]{1,0:T(8,128)(2,1)S(1)}, bf16[512,128]{1,0:T(8,128)(2,1)S(1)}, u32[]{:S(2)}, u32[]{:S(2)}) collective-permute-start(bf16[512,128]{1,0:T(8,128)(2,1)S(1)} %get-tuple-element.69), channel_id=1, source_target_pairs={{0,24},{8,16},{16,8},{24,0},{1,25},{9,17},{17,9},{25,1},{2,26},{10... | collective-permute-start | bytes 393224 | tf_op jit(solution)/shard_map/ppermute | solution.py:39
  55.5 10.4 %collective-permute-start.28 = (bf16[512,128]{1,0:T(8,128)(2,1)S(1)}, bf16[512,128]{1,0:T(8,128)(2,1)S(1)}, u32[]{:S(2)}, u32[]{:S(2)}) collective-permute-start(bf16[512,128]{1,0:T(8,128)(2,1)S(1)} %get-tuple-element.64), channel_id=1, source_target_pairs={{0,6},{1,7},{2,4},{3,5},{4,2},{5,3},{6,0},{7,1},{8,14},{9,15},{10,... | collective-permute-start | bytes 393224 | tf_op jit(solution)/shard_map/ppermute | solution.py:39
  58.2 7.7 %collective-permute-start.29 = (bf16[512,128]{1,0:T(8,128)(2,1)S(1)}, bf16[512,128]{1,0:T(8,128)(2,1)S(1)}, u32[]{:S(2)}, u32[]{:S(2)}) collective-permute-start(bf16[512,128]{1,0:T(8,128)(2,1)S(1)} %get-tuple-element.65), channel_id=1, source_target_pairs={{0,4},{1,5},{2,6},{3,7},{4,0},{5,1},{6,2},{7,3},{8,12},{9,13},{10,... | collective-permute-start | bytes 393224 | tf_op jit(solution)/shard_map/ppermute | solution.py:39
  58.5 7.4 %collective-permute-start.30 = (bf16[512,128]{1,0:T(8,128)(2,1)S(1)}, bf16[512,128]{1,0:T(8,128)(2,1)S(1)}, u32[]{:S(2)}, u32[]{:S(2)}) collective-permute-start(bf16[512,128]{1,0:T(8,128)(2,1)S(1)} %get-tuple-element.66), channel_id=1, source_target_pairs={{0,2},{1,3},{2,0},{3,1},{4,6},{5,7},{6,4},{7,5},{8,10},{9,11},{10,... | collective-permute-start | bytes 393224 | tf_op jit(solution)/shard_map/ppermute | solution.py:39
  66.1 8.6 %collective-permute-start.42 = (bf16[8,64,128]{2,1,0:T(8,128)(2,1)S(1)}, bf16[8,64,128]{2,1,0:T(8,128)(2,1)S(1)}, u32[]{:S(2)}, u32[]{:S(2)}) collective-permute-start(bf16[8,64,128]{2,1,0:T(8,128)(2,1)S(1)} %get-tuple-element.71.refs_2_.refs_3_), channel_id=1, source_target_pairs={{0,16},{8,24},{16,0},{24,8},{1,17},{9,25},{17,1},{25,9},{2,18},{10... | collective-permute-start | bytes 393224 | tf_op jit(solution)/shard_map/ppermute | solution.py:39
  68.7 5.8 %collective-permute-start.41 = (bf16[7,64,128]{2,1,0:T(8,128)(2,1)S(1)}, bf16[7,64,128]{2,1,0:T(8,128)(2,1)S(1)}, u32[]{:S(2)}, u32[]{:S(2)}) collective-permute-start(bf16[7,64,128]{2,1,0:T(8,128)(2,1)S(1)} %slice.22), channel_id=1, source_target_pairs={{0,8},{8,0},{16,24},{24,16},{1,9},{9,1},{17,25},{25,17},{2,10},{10... | collective-permute-start | bytes 344072 | tf_op jit(solution)/shard_map/ppermute | solution.py:39
  68.8 7.3 %collective-permute-start.34 = (bf16[8,64,128]{2,1,0:T(8,128)(2,1)S(1)}, bf16[8,64,128]{2,1,0:T(8,128)(2,1)S(1)}, u32[]{:S(2)}, u32[]{:S(2)}) collective-permute-start(bf16[8,64,128]{2,1,0:T(8,128)(2,1)S(1)} %get-tuple-element.71.refs_2_.refs_3_), channel_id=1, source_target_pairs={{0,6},{1,7},{2,4},{3,5},{4,2},{5,3},{6,0},{7,1},{8,14},{9,15},{10,... | collective-permute-start | bytes 393224 | tf_op jit(solution)/shard_map/ppermute | solution.py:39
  70.6 6.2 %collective-permute-start.35 = (bf16[8,64,128]{2,1,0:T(8,128)(2,1)S(1)}, bf16[8,64,128]{2,1,0:T(8,128)(2,1)S(1)}, u32[]{:S(2)}, u32[]{:S(2)}) collective-permute-start(bf16[8,64,128]{2,1,0:T(8,128)(2,1)S(1)} %get-tuple-element.71.refs_2_.refs_3_), channel_id=1, source_target_pairs={{0,4},{1,5},{2,6},{3,7},{4,0},{5,1},{6,2},{7,3},{8,12},{9,13},{10,... | collective-permute-start | bytes 393224 | tf_op jit(solution)/shard_map/ppermute | solution.py:39
  71.7 5.1 %collective-permute-start.36 = (bf16[8,64,128]{2,1,0:T(8,128)(2,1)S(1)}, bf16[8,64,128]{2,1,0:T(8,128)(2,1)S(1)}, u32[]{:S(2)}, u32[]{:S(2)}) collective-permute-start(bf16[8,64,128]{2,1,0:T(8,128)(2,1)S(1)} %get-tuple-element.71.refs_2_.refs_3_), channel_id=1, source_target_pairs={{0,2},{1,3},{2,0},{3,1},{4,6},{5,7},{6,4},{7,5},{8,10},{9,11},{10,... | collective-permute-start | bytes 393224 | tf_op jit(solution)/shard_map/ppermute | solution.py:39
  74.8 5.2 %collective-permute-start.43 = (bf16[9,64,128]{2,1,0:T(8,128)(2,1)S(1)}, bf16[9,64,128]{2,1,0:T(8,128)(2,1)S(1)}, u32[]{:S(2)}, u32[]{:S(2)}) collective-permute-start(bf16[9,64,128]{2,1,0:T(8,128)(2,1)S(1)} %pad_maximum_fusion.2), channel_id=1, source_target_pairs={{0,8},{8,0},{16,24},{24,16},{1,9},{9,1},{17,25},{25,17},{2,10},{10... | collective-permute-start | bytes 442376 | tf_op jit(solution)/shard_map/ppermute | solution.py:39
  75.8 1.6 %collective-permute-start.37 = (bf16[8,64,128]{2,1,0:T(8,128)(2,1)S(1)}, bf16[8,64,128]{2,1,0:T(8,128)(2,1)S(1)}, u32[]{:S(2)}, u32[]{:S(2)}) collective-permute-start(bf16[8,64,128]{2,1,0:T(8,128)(2,1)S(1)} %get-tuple-element.71.refs_2_.refs_3_), channel_id=1, source_target_pairs={{0,1},{1,0},{2,3},{3,2},{4,5},{5,4},{6,7},{7,6},{8,9},{9,8},{10,11... | collective-permute-start | bytes 393224 | tf_op jit(solution)/shard_map/ppermute | solution.py:39
  76.8 1.5 %collective-permute-start.40 = (bf16[8,64,128]{2,1,0:T(8,128)(2,1)S(1)}, bf16[8,64,128]{2,1,0:T(8,128)(2,1)S(1)}, u32[]{:S(2)}, u32[]{:S(2)}) collective-permute-start(bf16[8,64,128]{2,1,0:T(8,128)(2,1)S(1)} %collective-permute-done.36.refs_5_), channel_id=1, source_target_pairs={{0,1},{1,0},{2,3},{3,2},{4,5},{5,4},{6,7},{7,6},{8,9},{9,8},{10,11... | collective-permute-start | bytes 393224 | tf_op jit(solution)/shard_map/ppermute | solution.py:39
  82.4 4.7 %collective-permute-start.45 = (f32[40,128]{1,0:T(8,128)S(1)}, f32[40,128]{1,0:T(8,128)S(1)}, u32[]{:S(2)}, u32[]{:S(2)}) collective-permute-start(f32[40,128]{1,0:T(8,128)S(1)} %add.12), channel_id=1, source_target_pairs={{0,6},{1,7},{2,4},{3,5},{4,2},{5,3},{6,0},{7,1},{8,14},{9,15},{10,... | collective-permute-start | bytes 61448 | tf_op jit(solution)/shard_map/ppermute | solution.py:39
  83.6 3.8 %collective-permute-start.46 = (f32[40,128]{1,0:T(8,128)S(1)}, f32[40,128]{1,0:T(8,128)S(1)}, u32[]{:S(2)}, u32[]{:S(2)}) collective-permute-start(f32[40,128]{1,0:T(8,128)S(1)} %add.12), channel_id=1, source_target_pairs={{0,4},{1,5},{2,6},{3,7},{4,0},{5,1},{6,2},{7,3},{8,12},{9,13},{10,... | collective-permute-start | bytes 61448 | tf_op jit(solution)/shard_map/ppermute | solution.py:39
  85.1 3.8 %collective-permute-start.47 = (f32[40,128]{1,0:T(8,128)S(1)}, f32[40,128]{1,0:T(8,128)S(1)}, u32[]{:S(2)}, u32[]{:S(2)}) collective-permute-start(f32[40,128]{1,0:T(8,128)S(1)} %add.12), channel_id=1, source_target_pairs={{0,2},{1,3},{2,0},{3,1},{4,6},{5,7},{6,4},{7,5},{8,10},{9,11},{10,... | collective-permute-start | bytes 61448 | tf_op jit(solution)/shard_map/ppermute | solution.py:39
  88.8 5.6 %collective-permute-start.48 = (f32[40,128]{1,0:T(8,128)S(1)}, f32[40,128]{1,0:T(8,128)S(1)}, u32[]{:S(2)}, u32[]{:S(2)}) collective-permute-start(f32[40,128]{1,0:T(8,128)S(1)} %add_add_fusion.refs_1_), channel_id=1, source_target_pairs={{0,24},{8,16},{16,8},{24,0},{1,25},{9,17},{17,9},{25,1},{2,26},{10... | collective-permute-start | bytes 61448 | tf_op jit(solution)/shard_map/ppermute | solution.py:39
  90.9 4.8 %collective-permute-start.49 = (f32[40,128]{1,0:T(8,128)S(1)}, f32[40,128]{1,0:T(8,128)S(1)}, u32[]{:S(2)}, u32[]{:S(2)}) collective-permute-start(f32[40,128]{1,0:T(8,128)S(1)} %add_add_fusion.refs_1_), channel_id=1, source_target_pairs={{0,16},{8,24},{16,0},{24,8},{1,17},{9,25},{17,1},{25,9},{2,18},{10... | collective-permute-start | bytes 61448 | tf_op jit(solution)/shard_map/ppermute | solution.py:39
  91.6 4.1 %collective-permute-start.50 = (f32[40,128]{1,0:T(8,128)S(1)}, f32[40,128]{1,0:T(8,128)S(1)}, u32[]{:S(2)}, u32[]{:S(2)}) collective-permute-start(f32[40,128]{1,0:T(8,128)S(1)} %add_add_fusion.refs_1_), channel_id=1, source_target_pairs={{0,8},{8,0},{16,24},{24,16},{1,9},{9,1},{17,25},{25,17},{2,10},{10... | collective-permute-start | bytes 61448 | tf_op jit(solution)/shard_map/ppermute | solution.py:39
  (9 other events, 22.7 us)

commit v20 on v19

--- a/solution.py
+++ b/solution.py
@@ -304,6 +304,13 @@
     return tuple(lax.broadcasted_iota(jnp.int32, (n, n), axis) for axis in (0, 1))
 
 
+def refined_reciprocal(x):
+    y = pl.reciprocal(x, approx=True)
+    for _ in range(2):
+        y = y * (2.0 - x * y)
+    return y
+
+
 def inverse_factor(gram):
     n = gram.shape[0]
     row, col = square_index(n)
@@ -323,7 +330,7 @@
         forward, solved = bands[at], bands[at]
         solved_block = list(block)
         for s in range(8):
-            scale = 1.0 / pick(block[s], s)
+            scale = refined_reciprocal(pick(block[s], s))
             below = jnp.where(line > s, block[s], 0.0) * scale
             above = jnp.where(line < s, solved_block[s] * scale, 0.0)
             both = below + above

time: 99.7 us -> 100 us (level)
  transfers between devices with their start and end apart: 51 -> 51, of which waited for: 30 -> 29; matrix products, arithmetic and copies ran while one was open for 0% -> 0% of each run, Pallas kernels for 5% -> 5%
where the time goes in v20:
time: 100 us; the launch traced here: 99.9 us
  starting transfers between devices  53.8 us (54%)
  waiting for transfers between devices  28.2 us (28%)
  Pallas kernels  13.3 us (13%)
  local copies, waits for them, and re-layouts  3.65 us (4%)
    ppermute x51, starting transfers between devices, trade(): return lax.ppermute(part, axis, [(i, i ^ d) for i in range(n)])  53.8 us
    ppermute x51, waiting for transfers between devices, trade(): return lax.ppermute(part, axis, [(i, i ^ d) for i in range(n)])  28.2 us
    pallas_call x16, Pallas kernels, call(): pl.pallas_call(lambda *refs: kernel(*refs[len(after):]), out_shape=jax.tr...  13.3 us
    unnamed x12, local copies, waits for them, and re-layouts  3.54 us
  transfers between devices with their start and end apart: 51, of which 29 were waited for; matrix products, arithmetic and copies ran while one was open for 0% of the time, Pallas kernels for 5%

profile of v20, /device:TPU:0, one launch (start us, length us, event | category | flops | bytes accessed | tf_op | source)
XLA Modules:
  0.0 99.9 jit_solution(12905354577824516837)
XLA Ops:
  0.6 0.9 copy-done.2
  1.6 4.1 %collective-permute-start.8 = (bf16[8,64,128]{2,1,0:T(8,128)(2,1)S(1)}, bf16[8,64,128]{2,1,0:T(8,128)(2,1)S(1)}, u32[]{:S(2)}, u32[]{:S(2)}) collective-permute-start(bf16[8,64,128]{2,1,0:T(8,128)(2,1)S(1)} %shard_map.60.refs_2_.refs_3_), channel_id=1, source_target_pairs={{0,16},{8,24},{16,0},{24,8},{1,17},{9,25},{17,1},{25,9},{2,18},{10... | collective-permute-start | bytes 393224 | tf_op jit(solution)/shard_map/ppermute | solution.py:39
  5.7 1.6 %collective-permute-start.7 = (bf16[7,64,128]{2,1,0:T(8,128)(2,1)S(1)}, bf16[7,64,128]{2,1,0:T(8,128)(2,1)S(1)}, u32[]{:S(2)}, u32[]{:S(2)}) collective-permute-start(bf16[7,64,128]{2,1,0:T(8,128)(2,1)S(1)} %slice.24), channel_id=1, source_target_pairs={{0,8},{8,0},{16,24},{24,16},{1,9},{9,1},{17,25},{25,17},{2,10},{10... | collective-permute-start | bytes 344072 | tf_op jit(solution)/shard_map/ppermute | solution.py:39
  7.4 2.4 %collective-permute-start = (bf16[8,64,128]{2,1,0:T(8,128)(2,1)S(1)}, bf16[8,64,128]{2,1,0:T(8,128)(2,1)S(1)}, u32[]{:S(2)}, u32[]{:S(2)}) collective-permute-start(bf16[8,64,128]{2,1,0:T(8,128)(2,1)S(1)} %shard_map.60.refs_2_.refs_3_), channel_id=1, source_target_pairs={{0,6},{1,7},{2,4},{3,5},{4,2},{5,3},{6,0},{7,1},{8,14},{9,15},{10,... | collective-permute-start | bytes 393224 | tf_op jit(solution)/shard_map/ppermute | solution.py:39
  12.6 0.9 collective-permute-start.9
  14.0 1.7 %collective-permute-done.1.refs_4_ = bf16[8,64,128]{2,1,0:T(8,128)(2,1)S(1)} collective-permute-done((bf16[8,64,128]{2,1,0:T(8,128)(2,1)S(1)}, bf16[8,64,128]{2,1,0:T(8,128)(2,1)S(1)}, u32[]{:S(2)}, u32[]{:S(2)}) %collective-permute-start.1) | collective-permute-done | bytes 131104 | tf_op jit(solution)/shard_map/ppermute | solution.py:39
  16.3 0.8 collective-permute-done.5.refs_8_
  17.3 1.2 %copy-done = bf16[1,1,32,128,128]{4,3,2,1,0:T(8,128)(2,1)S(1)} copy-done((bf16[1,1,32,128,128]{4,3,2,1,0:T(8,128)(2,1)S(1)}, bf16[1,1,32,128,128]{4,3,2,1,0:T(8,128)(2,1)}, u32[]{:S(2)}) %copy-start) | copy-done | bytes 1048600
  18.5 1.1 %shard_map.62 = (f32[8,80,128]{2,1,0:T(8,128)S(1)}, f32[32,80,128]{2,1,0:T(8,128)S(1)}, bf16[528,128]{1,0:T(8,128)(2,1)S(1)}, bf16[528,128]{1,0:T(8,128)(2,1)S(1)}, bf16[528,128]{1,0:T(8,128)(2,1)S(1)}) custom-call(s32[3,32]{1,0:T(4,128)S(1)} %shard_map.59.refs_0_.refs_1_, bf16[32,128,128]{2,1,0:T(8,128)(2,1)S(1)} %bitcast.5, ...), custom_call_target="tpu_custom_call", output_to_operand_aliasing={{1}: (10, {})} | custom-call | flops 67108864 | bytes 3408256 | tf_op jit(solution)/shard_map/pallas_call | solution.py:25
  19.7 1.5 %shard_map.63 = (f32[64,80,128]{2,1,0:T(8,128)S(1)}, bf16[4,528,128]{2,1,0:T(8,128)(2,1)S(1)}) custom-call(f32[8,80,128]{2,1,0:T(8,128)S(1)} %get-tuple-element.39.refs_0_.refs_3_, s32[3,32]{1,0:T(4,128)S(1)} %shard_map.59.refs_0_.refs_1_, bf16[32,128,128]{2,1,0:T(8,128)(2,1)S(1)} %bitcast.6, ...), custom_call_target="tpu_custom_call", output_to_operand_aliasing={{0}: (7, {})} | custom-call | flops 67108864 | bytes 4194688 | tf_op jit(solution)/shard_map/pallas_call | solution.py:25
  22.1 1.5 %collective-permute-start.15 = (bf16[528,128]{1,0:T(8,128)(2,1)S(1)}, bf16[528,128]{1,0:T(8,128)(2,1)S(1)}, u32[]{:S(2)}, u32[]{:S(2)}) collective-permute-start(bf16[528,128]{1,0:T(8,128)(2,1)S(1)} %get-tuple-element.51), channel_id=1, source_target_pairs={{0,16},{8,24},{16,0},{24,8},{1,17},{9,25},{17,1},{25,9},{2,18},{10... | collective-permute-start | bytes 405512 | tf_op jit(solution)/shard_map/ppermute | solution.py:39
  23.6 2.4 %collective-permute-start.16 = (bf16[528,128]{1,0:T(8,128)(2,1)S(1)}, bf16[528,128]{1,0:T(8,128)(2,1)S(1)}, u32[]{:S(2)}, u32[]{:S(2)}) collective-permute-start(bf16[528,128]{1,0:T(8,128)(2,1)S(1)} %get-tuple-element.52), channel_id=1, source_target_pairs={{0,24},{8,16},{16,8},{24,0},{1,25},{9,17},{17,9},{25,1},{2,26},{10... | collective-permute-start | bytes 405512 | tf_op jit(solution)/shard_map/ppermute | solution.py:39
  26.1 1.8 %collective-permute-start.11 = (bf16[528,128]{1,0:T(8,128)(2,1)S(1)}, bf16[528,128]{1,0:T(8,128)(2,1)S(1)}, u32[]{:S(2)}, u32[]{:S(2)}) collective-permute-start(bf16[528,128]{1,0:T(8,128)(2,1)S(1)} %get-tuple-element.47), channel_id=1, source_target_pairs={{0,6},{1,7},{2,4},{3,5},{4,2},{5,3},{6,0},{7,1},{8,14},{9,15},{10,... | collective-permute-start | bytes 405512 | tf_op jit(solution)/shard_map/ppermute | solution.py:39
  28.0 1.2 %collective-permute-start.12 = (bf16[528,128]{1,0:T(8,128)(2,1)S(1)}, bf16[528,128]{1,0:T(8,128)(2,1)S(1)}, u32[]{:S(2)}, u32[]{:S(2)}) collective-permute-start(bf16[528,128]{1,0:T(8,128)(2,1)S(1)} %get-tuple-element.48), channel_id=1, source_target_pairs={{0,4},{1,5},{2,6},{3,7},{4,0},{5,1},{6,2},{7,3},{8,12},{9,13},{10,... | collective-permute-start | bytes 405512 | tf_op jit(solution)/shard_map/ppermute | solution.py:39
  29.4 1.5 %collective-permute-start.13 = (bf16[528,128]{1,0:T(8,128)(2,1)S(1)}, bf16[528,128]{1,0:T(8,128)(2,1)S(1)}, u32[]{:S(2)}, u32[]{:S(2)}) collective-permute-start(bf16[528,128]{1,0:T(8,128)(2,1)S(1)} %get-tuple-element.49), channel_id=1, source_target_pairs={{0,2},{1,3},{2,0},{3,1},{4,6},{5,7},{6,4},{7,5},{8,10},{9,11},{10,... | collective-permute-start | bytes 405512 | tf_op jit(solution)/shard_map/ppermute | solution.py:39
  30.9 4.4 %collective-permute-done.15.refs_8_ = bf16[528,128]{1,0:T(8,128)(2,1)S(1)} collective-permute-done((bf16[528,128]{1,0:T(8,128)(2,1)S(1)}, bf16[528,128]{1,0:T(8,128)(2,1)S(1)}, u32[]{:S(2)}, u32[]{:S(2)}) %collective-permute-start.15) | collective-permute-done | bytes 135200 | tf_op jit(solution)/shard_map/ppermute | solution.py:39
  35.5 3.0 %collective-permute-start.25 = (bf16[8,64,128]{2,1,0:T(8,128)(2,1)S(1)}, bf16[8,64,128]{2,1,0:T(8,128)(2,1)S(1)}, u32[]{:S(2)}, u32[]{:S(2)}) collective-permute-start(bf16[8,64,128]{2,1,0:T(8,128)(2,1)S(1)} %get-tuple-element.55.refs_2_.refs_3_), channel_id=1, source_target_pairs={{0,16},{8,24},{16,0},{24,8},{1,17},{9,25},{17,1},{25,9},{2,18},{10... | collective-permute-start | bytes 393224 | tf_op jit(solution)/shard_map/ppermute | solution.py:39
  38.6 2.5 %collective-permute-start.17 = (bf16[8,64,128]{2,1,0:T(8,128)(2,1)S(1)}, bf16[8,64,128]{2,1,0:T(8,128)(2,1)S(1)}, u32[]{:S(2)}, u32[]{:S(2)}) collective-permute-start(bf16[8,64,128]{2,1,0:T(8,128)(2,1)S(1)} %get-tuple-element.55.refs_2_.refs_3_), channel_id=1, source_target_pairs={{0,6},{1,7},{2,4},{3,5},{4,2},{5,3},{6,0},{7,1},{8,14},{9,15},{10,... | collective-permute-start | bytes 393224 | tf_op jit(solution)/shard_map/ppermute | solution.py:39
  42.3 1.7 %collective-permute-done.24.refs_5_ = bf16[7,64,128]{2,1,0:T(8,128)(2,1)S(1)} collective-permute-done((bf16[7,64,128]{2,1,0:T(8,128)(2,1)S(1)}, bf16[7,64,128]{2,1,0:T(8,128)(2,1)S(1)}, u32[]{:S(2)}, u32[]{:S(2)}) %collective-permute-start.24) | collective-permute-done | bytes 114720 | tf_op jit(solution)/shard_map/ppermute | solution.py:39
  44.2 1.3 %collective-permute-start.26 = (bf16[9,64,128]{2,1,0:T(8,128)(2,1)S(1)}, bf16[9,64,128]{2,1,0:T(8,128)(2,1)S(1)}, u32[]{:S(2)}, u32[]{:S(2)}) collective-permute-start(bf16[9,64,128]{2,1,0:T(8,128)(2,1)S(1)} %pad_maximum_fusion.1), channel_id=1, source_target_pairs={{0,8},{8,0},{16,24},{24,16},{1,9},{9,1},{17,25},{25,17},{2,10},{10... | collective-permute-start | bytes 442376 | tf_op jit(solution)/shard_map/ppermute | solution.py:39
  47.1 0.8 collective-permute-done.22.refs_8_
  48.1 1.0 %shard_map.67 = (f32[8,64,128]{2,1,0:T(8,128)S(1)}, f32[32,64,128]{2,1,0:T(8,128)S(1)}, bf16[512,128]{1,0:T(8,128)(2,1)S(1)}, bf16[512,128]{1,0:T(8,128)(2,1)S(1)}, bf16[512,128]{1,0:T(8,128)(2,1)S(1)}) custom-call(s32[3,32]{1,0:T(4,128)S(1)} %shard_map.59.refs_0_.refs_1_, bf16[32,128,128]{2,1,0:T(8,128)(2,1)S(1)} %bitcast.7, ...), custom_call_target="tpu_custom_call", output_to_operand_aliasing={{1}: (10, {})} | custom-call | flops 67108864 | bytes 3146112 | tf_op jit(solution)/shard_map/pallas_call | solution.py:25
  49.4 1.4 %shard_map.68 = (f32[64,64,128]{2,1,0:T(8,128)S(1)}, bf16[4,512,128]{2,1,0:T(8,128)(2,1)S(1)}) custom-call(f32[8,64,128]{2,1,0:T(8,128)S(1)} %get-tuple-element.57.refs_0_.refs_4_, s32[3,32]{1,0:T(4,128)S(1)} %shard_map.59.refs_0_.refs_1_, bf16[32,128,128]{2,1,0:T(8,128)(2,1)S(1)} %bitcast.8, ...), custom_call_target="tpu_custom_call", output_to_operand_aliasing={{0}: (7, {})} | custom-call | flops 67108864 | bytes 3670400 | tf_op jit(solution)/shard_map/pallas_call | solution.py:25
  51.0 2.0 %collective-permute-start.31 = (bf16[512,128]{1,0:T(8,128)(2,1)S(1)}, bf16[512,128]{1,0:T(8,128)(2,1)S(1)}, u32[]{:S(2)}, u32[]{:S(2)}) collective-permute-start(bf16[512,128]{1,0:T(8,128)(2,1)S(1)} %get-tuple-element.67), channel_id=1, source_target_pairs={{0,8},{8,0},{16,24},{24,16},{1,9},{9,1},{17,25},{25,17},{2,10},{10... | collective-permute-start | bytes 393224 | tf_op jit(solution)/shard_map/ppermute | solution.py:39
  53.5 1.8 %collective-permute-start.33 = (bf16[512,128]{1,0:T(8,128)(2,1)S(1)}, bf16[512,128]{1,0:T(8,128)(2,1)S(1)}, u32[]{:S(2)}, u32[]{:S(2)}) collective-permute-start(bf16[512,128]{1,0:T(8,128)(2,1)S(1)} %get-tuple-element.69), channel_id=1, source_target_pairs={{0,24},{8,16},{16,8},{24,0},{1,25},{9,17},{17,9},{25,1},{2,26},{10... | collective-permute-start | bytes 393224 | tf_op jit(solution)/shard_map/ppermute | solution.py:39
  55.5 2.7 %collective-permute-start.28 = (bf16[512,128]{1,0:T(8,128)(2,1)S(1)}, bf16[512,128]{1,0:T(8,128)(2,1)S(1)}, u32[]{:S(2)}, u32[]{:S(2)}) collective-permute-start(bf16[512,128]{1,0:T(8,128)(2,1)S(1)} %get-tuple-element.64), channel_id=1, source_target_pairs={{0,6},{1,7},{2,4},{3,5},{4,2},{5,3},{6,0},{7,1},{8,14},{9,15},{10,... | collective-permute-start | bytes 393224 | tf_op jit(solution)/shard_map/ppermute | solution.py:39
  58.5 1.7 %collective-permute-start.30 = (bf16[512,128]{1,0:T(8,128)(2,1)S(1)}, bf16[512,128]{1,0:T(8,128)(2,1)S(1)}, u32[]{:S(2)}, u32[]{:S(2)}) collective-permute-start(bf16[512,128]{1,0:T(8,128)(2,1)S(1)} %get-tuple-element.66), channel_id=1, source_target_pairs={{0,2},{1,3},{2,0},{3,1},{4,6},{5,7},{6,4},{7,5},{8,10},{9,11},{10,... | collective-permute-start | bytes 393224 | tf_op jit(solution)/shard_map/ppermute | solution.py:39
  60.2 5.7 %collective-permute-done.32.refs_9_ = bf16[512,128]{1,0:T(8,128)(2,1)S(1)} collective-permute-done((bf16[512,128]{1,0:T(8,128)(2,1)S(1)}, bf16[512,128]{1,0:T(8,128)(2,1)S(1)}, u32[]{:S(2)}, u32[]{:S(2)}) %collective-permute-start.32) | collective-permute-done | bytes 131104 | tf_op jit(solution)/shard_map/ppermute | solution.py:39
  66.1 2.5 %collective-permute-start.42 = (bf16[8,64,128]{2,1,0:T(8,128)(2,1)S(1)}, bf16[8,64,128]{2,1,0:T(8,128)(2,1)S(1)}, u32[]{:S(2)}, u32[]{:S(2)}) collective-permute-start(bf16[8,64,128]{2,1,0:T(8,128)(2,1)S(1)} %get-tuple-element.71.refs_2_.refs_3_), channel_id=1, source_target_pairs={{0,16},{8,24},{16,0},{24,8},{1,17},{9,25},{17,1},{25,9},{2,18},{10... | collective-permute-start | bytes 393224 | tf_op jit(solution)/shard_map/ppermute | solution.py:39
  68.8 1.9 %collective-permute-start.34 = (bf16[8,64,128]{2,1,0:T(8,128)(2,1)S(1)}, bf16[8,64,128]{2,1,0:T(8,128)(2,1)S(1)}, u32[]{:S(2)}, u32[]{:S(2)}) collective-permute-start(bf16[8,64,128]{2,1,0:T(8,128)(2,1)S(1)} %get-tuple-element.71.refs_2_.refs_3_), channel_id=1, source_target_pairs={{0,6},{1,7},{2,4},{3,5},{4,2},{5,3},{6,0},{7,1},{8,14},{9,15},{10,... | collective-permute-start | bytes 393224 | tf_op jit(solution)/shard_map/ppermute | solution.py:39
  70.6 1.1 %collective-permute-start.35 = (bf16[8,64,128]{2,1,0:T(8,128)(2,1)S(1)}, bf16[8,64,128]{2,1,0:T(8,128)(2,1)S(1)}, u32[]{:S(2)}, u32[]{:S(2)}) collective-permute-start(bf16[8,64,128]{2,1,0:T(8,128)(2,1)S(1)} %get-tuple-element.71.refs_2_.refs_3_), channel_id=1, source_target_pairs={{0,4},{1,5},{2,6},{3,7},{4,0},{5,1},{6,2},{7,3},{8,12},{9,13},{10,... | collective-permute-start | bytes 393224 | tf_op jit(solution)/shard_map/ppermute | solution.py:39
  73.0 1.5 %collective-permute-done.41.refs_5_ = bf16[7,64,128]{2,1,0:T(8,128)(2,1)S(1)} collective-permute-done((bf16[7,64,128]{2,1,0:T(8,128)(2,1)S(1)}, bf16[7,64,128]{2,1,0:T(8,128)(2,1)S(1)}, u32[]{:S(2)}, u32[]{:S(2)}) %collective-permute-start.41) | collective-permute-done | bytes 114720 | tf_op jit(solution)/shard_map/ppermute | solution.py:39
  74.8 1.0 collective-permute-start.43
  77.4 0.7 collective-permute-done.39.refs_8_
  78.3 1.0 shard_map.71.refs_1_
  80.0 1.2 %shard_map.73 = f32[40,128]{1,0:T(8,128)S(1)} custom-call(s32[3,32]{1,0:T(4,128)S(1)} %shard_map.59.refs_0_.refs_1_, bf16[64,4096]{1,0:T(8,128)(2,1)S(1)} %shard_map.71.refs_1_, f32[64,128]{1,0:T(8,128)S(1)} %shard_map.72.refs_2_, bf16[8,64,128]{2,1,0:T(8,128)(2,1)S(1)} %get-tuple-element.71.refs_2_.refs_3_, ...), custom_call_target="tpu_custom_call" | custom-call | flops 33554432 | bytes 1081728 | tf_op jit(solution)/shard_map/pallas_call | solution.py:25
  81.3 1.2 %collective-permute-done.44 = f32[40,128]{1,0:T(8,128)S(1)} collective-permute-done((f32[40,128]{1,0:T(8,128)S(1)}, f32[40,128]{1,0:T(8,128)S(1)}, u32[]{:S(2)}, u32[]{:S(2)}) %collective-permute-start.44) | collective-permute-done | bytes 20512 | tf_op jit(solution)/shard_map/ppermute | solution.py:39
  82.4 1.1 %collective-permute-start.45 = (f32[40,128]{1,0:T(8,128)S(1)}, f32[40,128]{1,0:T(8,128)S(1)}, u32[]{:S(2)}, u32[]{:S(2)}) collective-permute-start(f32[40,128]{1,0:T(8,128)S(1)} %add.12), channel_id=1, source_target_pairs={{0,6},{1,7},{2,4},{3,5},{4,2},{5,3},{6,0},{7,1},{8,14},{9,15},{10,... | collective-permute-start | bytes 61448 | tf_op jit(solution)/shard_map/ppermute | solution.py:39
  83.6 1.5 %collective-permute-start.46 = (f32[40,128]{1,0:T(8,128)S(1)}, f32[40,128]{1,0:T(8,128)S(1)}, u32[]{:S(2)}, u32[]{:S(2)}) collective-permute-start(f32[40,128]{1,0:T(8,128)S(1)} %add.12), channel_id=1, source_target_pairs={{0,4},{1,5},{2,6},{3,7},{4,0},{5,1},{6,2},{7,3},{8,12},{9,13},{10,... | collective-permute-start | bytes 61448 | tf_op jit(solution)/shard_map/ppermute | solution.py:39
  85.1 0.9 collective-permute-start.47
  85.9 1.2 %collective-permute-done.45 = f32[40,128]{1,0:T(8,128)S(1)} collective-permute-done((f32[40,128]{1,0:T(8,128)S(1)}, f32[40,128]{1,0:T(8,128)S(1)}, u32[]{:S(2)}, u32[]{:S(2)}) %collective-permute-start.45) | collective-permute-done | bytes 20512 | tf_op jit(solution)/shard_map/ppermute | solution.py:39
  87.3 1.5 %collective-permute-done.47 = f32[40,128]{1,0:T(8,128)S(1)} collective-permute-done((f32[40,128]{1,0:T(8,128)S(1)}, f32[40,128]{1,0:T(8,128)S(1)}, u32[]{:S(2)}, u32[]{:S(2)}) %collective-permute-start.47) | collective-permute-done | bytes 20512 | tf_op jit(solution)/shard_map/ppermute | solution.py:39
  88.8 2.0 %collective-permute-start.48 = (f32[40,128]{1,0:T(8,128)S(1)}, f32[40,128]{1,0:T(8,128)S(1)}, u32[]{:S(2)}, u32[]{:S(2)}) collective-permute-start(f32[40,128]{1,0:T(8,128)S(1)} %add_add_fusion.refs_1_), channel_id=1, source_target_pairs={{0,24},{8,16},{16,8},{24,0},{1,25},{9,17},{17,9},{25,1},{2,26},{10... | collective-permute-start | bytes 61448 | tf_op jit(solution)/shard_map/ppermute | solution.py:39
  90.9 0.7 collective-permute-start.49
  91.6 1.7 %collective-permute-start.50 = (f32[40,128]{1,0:T(8,128)S(1)}, f32[40,128]{1,0:T(8,128)S(1)}, u32[]{:S(2)}, u32[]{:S(2)}) collective-permute-start(f32[40,128]{1,0:T(8,128)S(1)} %add_add_fusion.refs_1_), channel_id=1, source_target_pairs={{0,8},{8,0},{16,24},{24,16},{1,9},{9,1},{17,25},{25,17},{2,10},{10... | collective-permute-start | bytes 61448 | tf_op jit(solution)/shard_map/ppermute | solution.py:39
  93.3 1.2 %collective-permute-done.48.refs_2_ = f32[40,128]{1,0:T(8,128)S(1)} collective-permute-done((f32[40,128]{1,0:T(8,128)S(1)}, f32[40,128]{1,0:T(8,128)S(1)}, u32[]{:S(2)}, u32[]{:S(2)}) %collective-permute-start.48) | collective-permute-done | bytes 20512 | tf_op jit(solution)/shard_map/ppermute | solution.py:39
  94.5 1.2 %collective-permute-done.49.refs_3_ = f32[40,128]{1,0:T(8,128)S(1)} collective-permute-done((f32[40,128]{1,0:T(8,128)S(1)}, f32[40,128]{1,0:T(8,128)S(1)}, u32[]{:S(2)}, u32[]{:S(2)}) %collective-permute-start.49) | collective-permute-done | bytes 20512 | tf_op jit(solution)/shard_map/ppermute | solution.py:39
  95.7 4.2 %shard_map.74 = (f32[64,1024]{1,0:T(8,128)}, f32[64,64]{1,0:T(8,128)}) custom-call(f32[64,1024]{1,0:T(8,128)S(1)} %get-tuple-element.70.refs_0_, f32[40,128]{1,0:T(8,128)S(1)} %add_add_fusion.refs_1_, f32[40,128]{1,0:T(8,128)S(1)} %collective-permute-done.48.refs_2_, f32[40,128]{1,0:T(8,128)S(1)} %collective-permute-done.49.refs_3_, ...), custom_call_target="tpu_custom_call" | custom-call | bytes 344064 | tf_op jit(solution)/shard_map/pallas_call | solution.py:25
  (95 shorter events, 14.8 us)
Async XLA Ops:
  1.6 11.0 %collective-permute-start.8 = (bf16[8,64,128]{2,1,0:T(8,128)(2,1)S(1)}, bf16[8,64,128]{2,1,0:T(8,128)(2,1)S(1)}, u32[]{:S(2)}, u32[]{:S(2)}) collective-permute-start(bf16[8,64,128]{2,1,0:T(8,128)(2,1)S(1)} %shard_map.60.refs_2_.refs_3_), channel_id=1, source_target_pairs={{0,16},{8,24},{16,0},{24,8},{1,17},{9,25},{17,1},{25,9},{2,18},{10... | collective-permute-start | bytes 393224 | tf_op jit(solution)/shard_map/ppermute | solution.py:39
  5.7 6.9 %collective-permute-start.7 = (bf16[7,64,128]{2,1,0:T(8,128)(2,1)S(1)}, bf16[7,64,128]{2,1,0:T(8,128)(2,1)S(1)}, u32[]{:S(2)}, u32[]{:S(2)}) collective-permute-start(bf16[7,64,128]{2,1,0:T(8,128)(2,1)S(1)} %slice.24), channel_id=1, source_target_pairs={{0,8},{8,0},{16,24},{24,16},{1,9},{9,1},{17,25},{25,17},{2,10},{10... | collective-permute-start | bytes 344072 | tf_op jit(solution)/shard_map/ppermute | solution.py:39
  7.4 6.6 %collective-permute-start = (bf16[8,64,128]{2,1,0:T(8,128)(2,1)S(1)}, bf16[8,64,128]{2,1,0:T(8,128)(2,1)S(1)}, u32[]{:S(2)}, u32[]{:S(2)}) collective-permute-start(bf16[8,64,128]{2,1,0:T(8,128)(2,1)S(1)} %shard_map.60.refs_2_.refs_3_), channel_id=1, source_target_pairs={{0,6},{1,7},{2,4},{3,5},{4,2},{5,3},{6,0},{7,1},{8,14},{9,15},{10,... | collective-permute-start | bytes 393224 | tf_op jit(solution)/shard_map/ppermute | solution.py:39
  9.8 5.9 %collective-permute-start.1 = (bf16[8,64,128]{2,1,0:T(8,128)(2,1)S(1)}, bf16[8,64,128]{2,1,0:T(8,128)(2,1)S(1)}, u32[]{:S(2)}, u32[]{:S(2)}) collective-permute-start(bf16[8,64,128]{2,1,0:T(8,128)(2,1)S(1)} %shard_map.60.refs_2_.refs_3_), channel_id=1, source_target_pairs={{0,4},{1,5},{2,6},{3,7},{4,0},{5,1},{6,2},{7,3},{8,12},{9,13},{10,... | collective-permute-start | bytes 393224 | tf_op jit(solution)/shard_map/ppermute | solution.py:39
  10.3 5.5 %collective-permute-start.2 = (bf16[8,64,128]{2,1,0:T(8,128)(2,1)S(1)}, bf16[8,64,128]{2,1,0:T(8,128)(2,1)S(1)}, u32[]{:S(2)}, u32[]{:S(2)}) collective-permute-start(bf16[8,64,128]{2,1,0:T(8,128)(2,1)S(1)} %shard_map.60.refs_2_.refs_3_), channel_id=1, source_target_pairs={{0,2},{1,3},{2,0},{3,1},{4,6},{5,7},{6,4},{7,5},{8,10},{9,11},{10,... | collective-permute-start | bytes 393224 | tf_op jit(solution)/shard_map/ppermute | solution.py:39
  12.6 7.0 %collective-permute-start.9 = (bf16[9,64,128]{2,1,0:T(8,128)(2,1)S(1)}, bf16[9,64,128]{2,1,0:T(8,128)(2,1)S(1)}, u32[]{:S(2)}, u32[]{:S(2)}) collective-permute-start(bf16[9,64,128]{2,1,0:T(8,128)(2,1)S(1)} %pad_maximum_fusion), channel_id=1, source_target_pairs={{0,8},{8,0},{16,24},{24,16},{1,9},{9,1},{17,25},{25,17},{2,10},{10... | collective-permute-start | bytes 442376 | tf_op jit(solution)/shard_map/ppermute | solution.py:39
  13.5 2.8 %collective-permute-start.3 = (bf16[8,64,128]{2,1,0:T(8,128)(2,1)S(1)}, bf16[8,64,128]{2,1,0:T(8,128)(2,1)S(1)}, u32[]{:S(2)}, u32[]{:S(2)}) collective-permute-start(bf16[8,64,128]{2,1,0:T(8,128)(2,1)S(1)} %shard_map.60.refs_2_.refs_3_), channel_id=1, source_target_pairs={{0,1},{1,0},{2,3},{3,2},{4,5},{5,4},{6,7},{7,6},{8,9},{9,8},{10,11... | collective-permute-start | bytes 393224 | tf_op jit(solution)/shard_map/ppermute | solution.py:39
  13.9 2.3 %collective-permute-start.4 = (bf16[8,64,128]{2,1,0:T(8,128)(2,1)S(1)}, bf16[8,64,128]{2,1,0:T(8,128)(2,1)S(1)}, u32[]{:S(2)}, u32[]{:S(2)}) collective-permute-start(bf16[8,64,128]{2,1,0:T(8,128)(2,1)S(1)} %collective-permute-done.refs_3_), channel_id=1, source_target_pairs={{0,1},{1,0},{2,3},{3,2},{4,5},{5,4},{6,7},{7,6},{8,9},{9,8},{10,11... | collective-permute-start | bytes 393224 | tf_op jit(solution)/shard_map/ppermute | solution.py:39
  15.7 1.3 %collective-permute-start.5 = (bf16[8,64,128]{2,1,0:T(8,128)(2,1)S(1)}, bf16[8,64,128]{2,1,0:T(8,128)(2,1)S(1)}, u32[]{:S(2)}, u32[]{:S(2)}) collective-permute-start(bf16[8,64,128]{2,1,0:T(8,128)(2,1)S(1)} %collective-permute-done.1.refs_4_), channel_id=1, source_target_pairs={{0,1},{1,0},{2,3},{3,2},{4,5},{5,4},{6,7},{7,6},{8,9},{9,8},{10,11... | collective-permute-start | bytes 393224 | tf_op jit(solution)/shard_map/ppermute | solution.py:39
  15.8 1.4 %collective-permute-start.6 = (bf16[8,64,128]{2,1,0:T(8,128)(2,1)S(1)}, bf16[8,64,128]{2,1,0:T(8,128)(2,1)S(1)}, u32[]{:S(2)}, u32[]{:S(2)}) collective-permute-start(bf16[8,64,128]{2,1,0:T(8,128)(2,1)S(1)} %collective-permute-done.2.refs_5_), channel_id=1, source_target_pairs={{0,1},{1,0},{2,3},{3,2},{4,5},{5,4},{6,7},{7,6},{8,9},{9,8},{10,11... | collective-permute-start | bytes 393224 | tf_op jit(solution)/shard_map/ppermute | solution.py:39
  21.2 4.8 %collective-permute-start.10 = (bf16[4,528,128]{2,1,0:T(8,128)(2,1)S(1)}, bf16[4,528,128]{2,1,0:T(8,128)(2,1)S(1)}, u32[]{:S(2)}, u32[]{:S(2)}) collective-permute-start(bf16[4,528,128]{2,1,0:T(8,128)(2,1)S(1)} %get-tuple-element.44), channel_id=1, source_target_pairs={{0,1},{1,0},{2,3},{3,2},{4,5},{5,4},{6,7},{7,6},{8,9},{9,8},{10,11... | collective-permute-start | bytes 1622024 | tf_op jit(solution)/shard_map/ppermute | solution.py:39
  21.6 7.8 %collective-permute-start.14 = (bf16[528,128]{1,0:T(8,128)(2,1)S(1)}, bf16[528,128]{1,0:T(8,128)(2,1)S(1)}, u32[]{:S(2)}, u32[]{:S(2)}) collective-permute-start(bf16[528,128]{1,0:T(8,128)(2,1)S(1)} %get-tuple-element.50), channel_id=1, source_target_pairs={{0,8},{8,0},{16,24},{24,16},{1,9},{9,1},{17,25},{25,17},{2,10},{10... | collective-permute-start | bytes 405512 | tf_op jit(solution)/shard_map/ppermute | solution.py:39
  22.1 13.2 %collective-permute-start.15 = (bf16[528,128]{1,0:T(8,128)(2,1)S(1)}, bf16[528,128]{1,0:T(8,128)(2,1)S(1)}, u32[]{:S(2)}, u32[]{:S(2)}) collective-permute-start(bf16[528,128]{1,0:T(8,128)(2,1)S(1)} %get-tuple-element.51), channel_id=1, source_target_pairs={{0,16},{8,24},{16,0},{24,8},{1,17},{9,25},{17,1},{25,9},{2,18},{10... | collective-permute-start | bytes 405512 | tf_op jit(solution)/shard_map/ppermute | solution.py:39
  23.6 11.6 %collective-permute-start.16 = (bf16[528,128]{1,0:T(8,128)(2,1)S(1)}, bf16[528,128]{1,0:T(8,128)(2,1)S(1)}, u32[]{:S(2)}, u32[]{:S(2)}) collective-permute-start(bf16[528,128]{1,0:T(8,128)(2,1)S(1)} %get-tuple-element.52), channel_id=1, source_target_pairs={{0,24},{8,16},{16,8},{24,0},{1,25},{9,17},{17,9},{25,1},{2,26},{10... | collective-permute-start | bytes 405512 | tf_op jit(solution)/shard_map/ppermute | solution.py:39
  26.1 9.1 %collective-permute-start.11 = (bf16[528,128]{1,0:T(8,128)(2,1)S(1)}, bf16[528,128]{1,0:T(8,128)(2,1)S(1)}, u32[]{:S(2)}, u32[]{:S(2)}) collective-permute-start(bf16[528,128]{1,0:T(8,128)(2,1)S(1)} %get-tuple-element.47), channel_id=1, source_target_pairs={{0,6},{1,7},{2,4},{3,5},{4,2},{5,3},{6,0},{7,1},{8,14},{9,15},{10,... | collective-permute-start | bytes 405512 | tf_op jit(solution)/shard_map/ppermute | solution.py:39
  28.0 7.3 %collective-permute-start.12 = (bf16[528,128]{1,0:T(8,128)(2,1)S(1)}, bf16[528,128]{1,0:T(8,128)(2,1)S(1)}, u32[]{:S(2)}, u32[]{:S(2)}) collective-permute-start(bf16[528,128]{1,0:T(8,128)(2,1)S(1)} %get-tuple-element.48), channel_id=1, source_target_pairs={{0,4},{1,5},{2,6},{3,7},{4,0},{5,1},{6,2},{7,3},{8,12},{9,13},{10,... | collective-permute-start | bytes 405512 | tf_op jit(solution)/shard_map/ppermute | solution.py:39
  29.4 5.9 %collective-permute-start.13 = (bf16[528,128]{1,0:T(8,128)(2,1)S(1)}, bf16[528,128]{1,0:T(8,128)(2,1)S(1)}, u32[]{:S(2)}, u32[]{:S(2)}) collective-permute-start(bf16[528,128]{1,0:T(8,128)(2,1)S(1)} %get-tuple-element.49), channel_id=1, source_target_pairs={{0,2},{1,3},{2,0},{3,1},{4,6},{5,7},{6,4},{7,5},{8,10},{9,11},{10,... | collective-permute-start | bytes 405512 | tf_op jit(solution)/shard_map/ppermute | solution.py:39
  35.5 8.7 %collective-permute-start.25 = (bf16[8,64,128]{2,1,0:T(8,128)(2,1)S(1)}, bf16[8,64,128]{2,1,0:T(8,128)(2,1)S(1)}, u32[]{:S(2)}, u32[]{:S(2)}) collective-permute-start(bf16[8,64,128]{2,1,0:T(8,128)(2,1)S(1)} %get-tuple-element.55.refs_2_.refs_3_), channel_id=1, source_target_pairs={{0,16},{8,24},{16,0},{24,8},{1,17},{9,25},{17,1},{25,9},{2,18},{10... | collective-permute-start | bytes 393224 | tf_op jit(solution)/shard_map/ppermute | solution.py:39
  38.5 5.5 %collective-permute-start.24 = (bf16[7,64,128]{2,1,0:T(8,128)(2,1)S(1)}, bf16[7,64,128]{2,1,0:T(8,128)(2,1)S(1)}, u32[]{:S(2)}, u32[]{:S(2)}) collective-permute-start(bf16[7,64,128]{2,1,0:T(8,128)(2,1)S(1)} %slice.20), channel_id=1, source_target_pairs={{0,8},{8,0},{16,24},{24,16},{1,9},{9,1},{17,25},{25,17},{2,10},{10... | collective-permute-start | bytes 344072 | tf_op jit(solution)/shard_map/ppermute | solution.py:39
  38.6 7.0 %collective-permute-start.17 = (bf16[8,64,128]{2,1,0:T(8,128)(2,1)S(1)}, bf16[8,64,128]{2,1,0:T(8,128)(2,1)S(1)}, u32[]{:S(2)}, u32[]{:S(2)}) collective-permute-start(bf16[8,64,128]{2,1,0:T(8,128)(2,1)S(1)} %get-tuple-element.55.refs_2_.refs_3_), channel_id=1, source_target_pairs={{0,6},{1,7},{2,4},{3,5},{4,2},{5,3},{6,0},{7,1},{8,14},{9,15},{10,... | collective-permute-start | bytes 393224 | tf_op jit(solution)/shard_map/ppermute | solution.py:39
  41.0 5.5 %collective-permute-start.18 = (bf16[8,64,128]{2,1,0:T(8,128)(2,1)S(1)}, bf16[8,64,128]{2,1,0:T(8,128)(2,1)S(1)}, u32[]{:S(2)}, u32[]{:S(2)}) collective-permute-start(bf16[8,64,128]{2,1,0:T(8,128)(2,1)S(1)} %get-tuple-element.55.refs_2_.refs_3_), channel_id=1, source_target_pairs={{0,4},{1,5},{2,6},{3,7},{4,0},{5,1},{6,2},{7,3},{8,12},{9,13},{10,... | collective-permute-start | bytes 393224 | tf_op jit(solution)/shard_map/ppermute | solution.py:39
  41.6 5.1 %collective-permute-start.19 = (bf16[8,64,128]{2,1,0:T(8,128)(2,1)S(1)}, bf16[8,64,128]{2,1,0:T(8,128)(2,1)S(1)}, u32[]{:S(2)}, u32[]{:S(2)}) collective-permute-start(bf16[8,64,128]{2,1,0:T(8,128)(2,1)S(1)} %get-tuple-element.55.refs_2_.refs_3_), channel_id=1, source_target_pairs={{0,2},{1,3},{2,0},{3,1},{4,6},{5,7},{6,4},{7,5},{8,10},{9,11},{10,... | collective-permute-start | bytes 393224 | tf_op jit(solution)/shard_map/ppermute | solution.py:39
  44.2 5.2 %collective-permute-start.26 = (bf16[9,64,128]{2,1,0:T(8,128)(2,1)S(1)}, bf16[9,64,128]{2,1,0:T(8,128)(2,1)S(1)}, u32[]{:S(2)}, u32[]{:S(2)}) collective-permute-start(bf16[9,64,128]{2,1,0:T(8,128)(2,1)S(1)} %pad_maximum_fusion.1), channel_id=1, source_target_pairs={{0,8},{8,0},{16,24},{24,16},{1,9},{9,1},{17,25},{25,17},{2,10},{10... | collective-permute-start | bytes 442376 | tf_op jit(solution)/shard_map/ppermute | solution.py:39
  45.5 1.6 %collective-permute-start.20 = (bf16[8,64,128]{2,1,0:T(8,128)(2,1)S(1)}, bf16[8,64,128]{2,1,0:T(8,128)(2,1)S(1)}, u32[]{:S(2)}, u32[]{:S(2)}) collective-permute-start(bf16[8,64,128]{2,1,0:T(8,128)(2,1)S(1)} %get-tuple-element.55.refs_2_.refs_3_), channel_id=1, source_target_pairs={{0,1},{1,0},{2,3},{3,2},{4,5},{5,4},{6,7},{7,6},{8,9},{9,8},{10,11... | collective-permute-start | bytes 393224 | tf_op jit(solution)/shard_map/ppermute | solution.py:39
  45.5 1.5 %collective-permute-start.21 = (bf16[8,64,128]{2,1,0:T(8,128)(2,1)S(1)}, bf16[8,64,128]{2,1,0:T(8,128)(2,1)S(1)}, u32[]{:S(2)}, u32[]{:S(2)}) collective-permute-start(bf16[8,64,128]{2,1,0:T(8,128)(2,1)S(1)} %collective-permute-done.17.refs_3_), channel_id=1, source_target_pairs={{0,1},{1,0},{2,3},{3,2},{4,5},{5,4},{6,7},{7,6},{8,9},{9,8},{10,11... | collective-permute-start | bytes 393224 | tf_op jit(solution)/shard_map/ppermute | solution.py:39
  46.5 1.3 %collective-permute-start.22 = (bf16[8,64,128]{2,1,0:T(8,128)(2,1)S(1)}, bf16[8,64,128]{2,1,0:T(8,128)(2,1)S(1)}, u32[]{:S(2)}, u32[]{:S(2)}) collective-permute-start(bf16[8,64,128]{2,1,0:T(8,128)(2,1)S(1)} %collective-permute-done.18.refs_4_), channel_id=1, source_target_pairs={{0,1},{1,0},{2,3},{3,2},{4,5},{5,4},{6,7},{7,6},{8,9},{9,8},{10,11... | collective-permute-start | bytes 393224 | tf_op jit(solution)/shard_map/ppermute | solution.py:39
  46.6 1.4 %collective-permute-start.23 = (bf16[8,64,128]{2,1,0:T(8,128)(2,1)S(1)}, bf16[8,64,128]{2,1,0:T(8,128)(2,1)S(1)}, u32[]{:S(2)}, u32[]{:S(2)}) collective-permute-start(bf16[8,64,128]{2,1,0:T(8,128)(2,1)S(1)} %collective-permute-done.19.refs_5_), channel_id=1, source_target_pairs={{0,1},{1,0},{2,3},{3,2},{4,5},{5,4},{6,7},{7,6},{8,9},{9,8},{10,11... | collective-permute-start | bytes 393224 | tf_op jit(solution)/shard_map/ppermute | solution.py:39
  50.9 4.5 %collective-permute-start.27 = (bf16[4,512,128]{2,1,0:T(8,128)(2,1)S(1)}, bf16[4,512,128]{2,1,0:T(8,128)(2,1)S(1)}, u32[]{:S(2)}, u32[]{:S(2)}) collective-permute-start(bf16[4,512,128]{2,1,0:T(8,128)(2,1)S(1)} %get-tuple-element.62), channel_id=1, source_target_pairs={{0,1},{1,0},{2,3},{3,2},{4,5},{5,4},{6,7},{7,6},{8,9},{9,8},{10,11... | collective-permute-start | bytes 1572872 | tf_op jit(solution)/shard_map/ppermute | solution.py:39
  51.0 7.6 %collective-permute-start.31 = (bf16[512,128]{1,0:T(8,128)(2,1)S(1)}, bf16[512,128]{1,0:T(8,128)(2,1)S(1)}, u32[]{:S(2)}, u32[]{:S(2)}) collective-permute-start(bf16[512,128]{1,0:T(8,128)(2,1)S(1)} %get-tuple-element.67), channel_id=1, source_target_pairs={{0,8},{8,0},{16,24},{24,16},{1,9},{9,1},{17,25},{25,17},{2,10},{10... | collective-permute-start | bytes 393224 | tf_op jit(solution)/shard_map/ppermute | solution.py:39
  53.0 12.9 %collective-permute-start.32 = (bf16[512,128]{1,0:T(8,128)(2,1)S(1)}, bf16[512,128]{1,0:T(8,128)(2,1)S(1)}, u32[]{:S(2)}, u32[]{:S(2)}) collective-permute-start(bf16[512,128]{1,0:T(8,128)(2,1)S(1)} %get-tuple-element.68), channel_id=1, source_target_pairs={{0,16},{8,24},{16,0},{24,8},{1,17},{9,25},{17,1},{25,9},{2,18},{10... | collective-permute-start | bytes 393224 | tf_op jit(solution)/shard_map/ppermute | solution.py:39
  53.5 12.4 %collective-permute-start.33 = (bf16[512,128]{1,0:T(8,128)(2,1)S(1)}, bf16[512,128]{1,0:T(8,128)(2,1)S(1)}, u32[]{:S(2)}, u32[]{:S(2)}) collective-permute-start(bf16[512,128]{1,0:T(8,128)(2,1)S(1)} %get-tuple-element.69), channel_id=1, source_target_pairs={{0,24},{8,16},{16,8},{24,0},{1,25},{9,17},{17,9},{25,1},{2,26},{10... | collective-permute-start | bytes 393224 | tf_op jit(solution)/shard_map/ppermute | solution.py:39
  55.5 10.4 %collective-permute-start.28 = (bf16[512,128]{1,0:T(8,128)(2,1)S(1)}, bf16[512,128]{1,0:T(8,128)(2,1)S(1)}, u32[]{:S(2)}, u32[]{:S(2)}) collective-permute-start(bf16[512,128]{1,0:T(8,128)(2,1)S(1)} %get-tuple-element.64), channel_id=1, source_target_pairs={{0,6},{1,7},{2,4},{3,5},{4,2},{5,3},{6,0},{7,1},{8,14},{9,15},{10,... | collective-permute-start | bytes 393224 | tf_op jit(solution)/shard_map/ppermute | solution.py:39
  58.2 7.7 %collective-permute-start.29 = (bf16[512,128]{1,0:T(8,128)(2,1)S(1)}, bf16[512,128]{1,0:T(8,128)(2,1)S(1)}, u32[]{:S(2)}, u32[]{:S(2)}) collective-permute-start(bf16[512,128]{1,0:T(8,128)(2,1)S(1)} %get-tuple-element.65), channel_id=1, source_target_pairs={{0,4},{1,5},{2,6},{3,7},{4,0},{5,1},{6,2},{7,3},{8,12},{9,13},{10,... | collective-permute-start | bytes 393224 | tf_op jit(solution)/shard_map/ppermute | solution.py:39
  58.5 7.4 %collective-permute-start.30 = (bf16[512,128]{1,0:T(8,128)(2,1)S(1)}, bf16[512,128]{1,0:T(8,128)(2,1)S(1)}, u32[]{:S(2)}, u32[]{:S(2)}) collective-permute-start(bf16[512,128]{1,0:T(8,128)(2,1)S(1)} %get-tuple-element.66), channel_id=1, source_target_pairs={{0,2},{1,3},{2,0},{3,1},{4,6},{5,7},{6,4},{7,5},{8,10},{9,11},{10,... | collective-permute-start | bytes 393224 | tf_op jit(solution)/shard_map/ppermute | solution.py:39
  66.1 8.6 %collective-permute-start.42 = (bf16[8,64,128]{2,1,0:T(8,128)(2,1)S(1)}, bf16[8,64,128]{2,1,0:T(8,128)(2,1)S(1)}, u32[]{:S(2)}, u32[]{:S(2)}) collective-permute-start(bf16[8,64,128]{2,1,0:T(8,128)(2,1)S(1)} %get-tuple-element.71.refs_2_.refs_3_), channel_id=1, source_target_pairs={{0,16},{8,24},{16,0},{24,8},{1,17},{9,25},{17,1},{25,9},{2,18},{10... | collective-permute-start | bytes 393224 | tf_op jit(solution)/shard_map/ppermute | solution.py:39
  68.7 5.8 %collective-permute-start.41 = (bf16[7,64,128]{2,1,0:T(8,128)(2,1)S(1)}, bf16[7,64,128]{2,1,0:T(8,128)(2,1)S(1)}, u32[]{:S(2)}, u32[]{:S(2)}) collective-permute-start(bf16[7,64,128]{2,1,0:T(8,128)(2,1)S(1)} %slice.22), channel_id=1, source_target_pairs={{0,8},{8,0},{16,24},{24,16},{1,9},{9,1},{17,25},{25,17},{2,10},{10... | collective-permute-start | bytes 344072 | tf_op jit(solution)/shard_map/ppermute | solution.py:39
  68.8 7.3 %collective-permute-start.34 = (bf16[8,64,128]{2,1,0:T(8,128)(2,1)S(1)}, bf16[8,64,128]{2,1,0:T(8,128)(2,1)S(1)}, u32[]{:S(2)}, u32[]{:S(2)}) collective-permute-start(bf16[8,64,128]{2,1,0:T(8,128)(2,1)S(1)} %get-tuple-element.71.refs_2_.refs_3_), channel_id=1, source_target_pairs={{0,6},{1,7},{2,4},{3,5},{4,2},{5,3},{6,0},{7,1},{8,14},{9,15},{10,... | collective-permute-start | bytes 393224 | tf_op jit(solution)/shard_map/ppermute | solution.py:39
  70.6 6.2 %collective-permute-start.35 = (bf16[8,64,128]{2,1,0:T(8,128)(2,1)S(1)}, bf16[8,64,128]{2,1,0:T(8,128)(2,1)S(1)}, u32[]{:S(2)}, u32[]{:S(2)}) collective-permute-start(bf16[8,64,128]{2,1,0:T(8,128)(2,1)S(1)} %get-tuple-element.71.refs_2_.refs_3_), channel_id=1, source_target_pairs={{0,4},{1,5},{2,6},{3,7},{4,0},{5,1},{6,2},{7,3},{8,12},{9,13},{10,... | collective-permute-start | bytes 393224 | tf_op jit(solution)/shard_map/ppermute | solution.py:39
  71.7 5.1 %collective-permute-start.36 = (bf16[8,64,128]{2,1,0:T(8,128)(2,1)S(1)}, bf16[8,64,128]{2,1,0:T(8,128)(2,1)S(1)}, u32[]{:S(2)}, u32[]{:S(2)}) collective-permute-start(bf16[8,64,128]{2,1,0:T(8,128)(2,1)S(1)} %get-tuple-element.71.refs_2_.refs_3_), channel_id=1, source_target_pairs={{0,2},{1,3},{2,0},{3,1},{4,6},{5,7},{6,4},{7,5},{8,10},{9,11},{10,... | collective-permute-start | bytes 393224 | tf_op jit(solution)/shard_map/ppermute | solution.py:39
  74.8 5.2 %collective-permute-start.43 = (bf16[9,64,128]{2,1,0:T(8,128)(2,1)S(1)}, bf16[9,64,128]{2,1,0:T(8,128)(2,1)S(1)}, u32[]{:S(2)}, u32[]{:S(2)}) collective-permute-start(bf16[9,64,128]{2,1,0:T(8,128)(2,1)S(1)} %pad_maximum_fusion.2), channel_id=1, source_target_pairs={{0,8},{8,0},{16,24},{24,16},{1,9},{9,1},{17,25},{25,17},{2,10},{10... | collective-permute-start | bytes 442376 | tf_op jit(solution)/shard_map/ppermute | solution.py:39
  75.8 1.6 %collective-permute-start.37 = (bf16[8,64,128]{2,1,0:T(8,128)(2,1)S(1)}, bf16[8,64,128]{2,1,0:T(8,128)(2,1)S(1)}, u32[]{:S(2)}, u32[]{:S(2)}) collective-permute-start(bf16[8,64,128]{2,1,0:T(8,128)(2,1)S(1)} %get-tuple-element.71.refs_2_.refs_3_), channel_id=1, source_target_pairs={{0,1},{1,0},{2,3},{3,2},{4,5},{5,4},{6,7},{7,6},{8,9},{9,8},{10,11... | collective-permute-start | bytes 393224 | tf_op jit(solution)/shard_map/ppermute | solution.py:39
  76.8 1.5 %collective-permute-start.40 = (bf16[8,64,128]{2,1,0:T(8,128)(2,1)S(1)}, bf16[8,64,128]{2,1,0:T(8,128)(2,1)S(1)}, u32[]{:S(2)}, u32[]{:S(2)}) collective-permute-start(bf16[8,64,128]{2,1,0:T(8,128)(2,1)S(1)} %collective-permute-done.36.refs_5_), channel_id=1, source_target_pairs={{0,1},{1,0},{2,3},{3,2},{4,5},{5,4},{6,7},{7,6},{8,9},{9,8},{10,11... | collective-permute-start | bytes 393224 | tf_op jit(solution)/shard_map/ppermute | solution.py:39
  82.4 4.7 %collective-permute-start.45 = (f32[40,128]{1,0:T(8,128)S(1)}, f32[40,128]{1,0:T(8,128)S(1)}, u32[]{:S(2)}, u32[]{:S(2)}) collective-permute-start(f32[40,128]{1,0:T(8,128)S(1)} %add.12), channel_id=1, source_target_pairs={{0,6},{1,7},{2,4},{3,5},{4,2},{5,3},{6,0},{7,1},{8,14},{9,15},{10,... | collective-permute-start | bytes 61448 | tf_op jit(solution)/shard_map/ppermute | solution.py:39
  83.6 3.8 %collective-permute-start.46 = (f32[40,128]{1,0:T(8,128)S(1)}, f32[40,128]{1,0:T(8,128)S(1)}, u32[]{:S(2)}, u32[]{:S(2)}) collective-permute-start(f32[40,128]{1,0:T(8,128)S(1)} %add.12), channel_id=1, source_target_pairs={{0,4},{1,5},{2,6},{3,7},{4,0},{5,1},{6,2},{7,3},{8,12},{9,13},{10,... | collective-permute-start | bytes 61448 | tf_op jit(solution)/shard_map/ppermute | solution.py:39
  85.1 3.8 %collective-permute-start.47 = (f32[40,128]{1,0:T(8,128)S(1)}, f32[40,128]{1,0:T(8,128)S(1)}, u32[]{:S(2)}, u32[]{:S(2)}) collective-permute-start(f32[40,128]{1,0:T(8,128)S(1)} %add.12), channel_id=1, source_target_pairs={{0,2},{1,3},{2,0},{3,1},{4,6},{5,7},{6,4},{7,5},{8,10},{9,11},{10,... | collective-permute-start | bytes 61448 | tf_op jit(solution)/shard_map/ppermute | solution.py:39
  88.8 5.6 %collective-permute-start.48 = (f32[40,128]{1,0:T(8,128)S(1)}, f32[40,128]{1,0:T(8,128)S(1)}, u32[]{:S(2)}, u32[]{:S(2)}) collective-permute-start(f32[40,128]{1,0:T(8,128)S(1)} %add_add_fusion.refs_1_), channel_id=1, source_target_pairs={{0,24},{8,16},{16,8},{24,0},{1,25},{9,17},{17,9},{25,1},{2,26},{10... | collective-permute-start | bytes 61448 | tf_op jit(solution)/shard_map/ppermute | solution.py:39
  90.9 4.9 %collective-permute-start.49 = (f32[40,128]{1,0:T(8,128)S(1)}, f32[40,128]{1,0:T(8,128)S(1)}, u32[]{:S(2)}, u32[]{:S(2)}) collective-permute-start(f32[40,128]{1,0:T(8,128)S(1)} %add_add_fusion.refs_1_), channel_id=1, source_target_pairs={{0,16},{8,24},{16,0},{24,8},{1,17},{9,25},{17,1},{25,9},{2,18},{10... | collective-permute-start | bytes 61448 | tf_op jit(solution)/shard_map/ppermute | solution.py:39
  91.6 4.1 %collective-permute-start.50 = (f32[40,128]{1,0:T(8,128)S(1)}, f32[40,128]{1,0:T(8,128)S(1)}, u32[]{:S(2)}, u32[]{:S(2)}) collective-permute-start(f32[40,128]{1,0:T(8,128)S(1)} %add_add_fusion.refs_1_), channel_id=1, source_target_pairs={{0,8},{8,0},{16,24},{24,16},{1,9},{9,1},{17,25},{25,17},{2,10},{10... | collective-permute-start | bytes 61448 | tf_op jit(solution)/shard_map/ppermute | solution.py:39
  (9 other events, 22.7 us)

commit v21 on v19

--- a/solution.py
+++ b/solution.py
@@ -97,6 +97,10 @@
     return jnp.concatenate(
         [total[start + k, vectors_n : vectors_n + 1, :] for k in range(group)], 0
     )
+
+
+def hold_kernel(tiles_ref, held_ref):
+    held_ref[...] = tiles_ref[...]
 
 
 def zero_kernel(*refs):
@@ -445,6 +449,14 @@
         16,
         [meta, tile_rows[None], tile_cols[None]],
     )
+    tiles = call(
+        hold_kernel,
+        jax.ShapeDtypeStruct(tiles.shape, BF16),
+        [],
+        16,
+        [tiles],
+        4 * tiles.size * DEGREE_ROWS,
+    )
     first, rounded, degree = call(
         functools.partial(first_kernel, chips_n),
         [vector_shape, rounded_shape, degree_shape],

time: 99.7 us -> 99.3 us (level)
  waiting for transfers between devices: 28.2 us -> 27 us
    ppermute x51, waiting for transfers between devices: 28.2 us -> 27 us  [trade(): return lax.ppermute(part, axis, [(i, i ^ d) for i in range(n)])]
    pallas_call x16 -> x17, Pallas kernels: 12.8 us -> 12.9 us  [call(): pl.pallas_call(lambda *refs: kernel(*refs[len(after):]), out_shape=jax.tr...]
    unnamed x12 -> x10, local copies, waits for them, and re-layouts: 3.54 us -> 3.49 us
  transfers between devices with their start and end apart: 51 -> 51, of which waited for: 30 -> 25; matrix products, arithmetic and copies ran while one was open for 0% -> 0% of each run, Pallas kernels for 5% -> 5%
where the time goes in v21:
time: 99.3 us; the launch traced here: 99.2 us
  starting transfers between devices  54.6 us (55%)
  waiting for transfers between devices  27 us (27%)
  Pallas kernels  12.9 us (13%)
  local copies, waits for them, and re-layouts  3.59 us (4%)
    ppermute x51, starting transfers between devices, trade(): return lax.ppermute(part, axis, [(i, i ^ d) for i in range(n)])  54.6 us
    ppermute x51, waiting for transfers between devices, trade(): return lax.ppermute(part, axis, [(i, i ^ d) for i in range(n)])  27 us
    pallas_call x17, Pallas kernels, call(): pl.pallas_call(lambda *refs: kernel(*refs[len(after):]), out_shape=jax.tr...  12.9 us
    unnamed x10, local copies, waits for them, and re-layouts  3.49 us
  transfers between devices with their start and end apart: 51, of which 25 were waited for; matrix products, arithmetic and copies ran while one was open for 0% of the time, Pallas kernels for 5%

profile of v21, /device:TPU:0, one launch (start us, length us, event | category | flops | bytes accessed | tf_op | source)
XLA Modules:
  0.0 99.2 jit_solution(9189427340378258486)
XLA Ops:
  0.6 0.9 copy-done
  1.6 4.1 %collective-permute-start.8 = (bf16[8,64,128]{2,1,0:T(8,128)(2,1)S(1)}, bf16[8,64,128]{2,1,0:T(8,128)(2,1)S(1)}, u32[]{:S(2)}, u32[]{:S(2)}) collective-permute-start(bf16[8,64,128]{2,1,0:T(8,128)(2,1)S(1)} %shard_map.61.refs_2_.refs_3_), channel_id=1, source_target_pairs={{0,16},{8,24},{16,0},{24,8},{1,17},{9,25},{17,1},{25,9},{2,18},{10... | collective-permute-start | bytes 393224 | tf_op jit(solution)/shard_map/ppermute | solution.py:39
  5.7 1.6 %collective-permute-start.7 = (bf16[7,64,128]{2,1,0:T(8,128)(2,1)S(1)}, bf16[7,64,128]{2,1,0:T(8,128)(2,1)S(1)}, u32[]{:S(2)}, u32[]{:S(2)}) collective-permute-start(bf16[7,64,128]{2,1,0:T(8,128)(2,1)S(1)} %slice.24), channel_id=1, source_target_pairs={{0,8},{8,0},{16,24},{24,16},{1,9},{9,1},{17,25},{25,17},{2,10},{10... | collective-permute-start | bytes 344072 | tf_op jit(solution)/shard_map/ppermute | solution.py:39
  7.4 2.4 %collective-permute-start = (bf16[8,64,128]{2,1,0:T(8,128)(2,1)S(1)}, bf16[8,64,128]{2,1,0:T(8,128)(2,1)S(1)}, u32[]{:S(2)}, u32[]{:S(2)}) collective-permute-start(bf16[8,64,128]{2,1,0:T(8,128)(2,1)S(1)} %shard_map.61.refs_2_.refs_3_), channel_id=1, source_target_pairs={{0,6},{1,7},{2,4},{3,5},{4,2},{5,3},{6,0},{7,1},{8,14},{9,15},{10,... | collective-permute-start | bytes 393224 | tf_op jit(solution)/shard_map/ppermute | solution.py:39
  12.6 0.9 collective-permute-start.9
  14.0 1.7 %collective-permute-done.1.refs_4_ = bf16[8,64,128]{2,1,0:T(8,128)(2,1)S(1)} collective-permute-done((bf16[8,64,128]{2,1,0:T(8,128)(2,1)S(1)}, bf16[8,64,128]{2,1,0:T(8,128)(2,1)S(1)}, u32[]{:S(2)}, u32[]{:S(2)}) %collective-permute-start.1) | collective-permute-done | bytes 131104 | tf_op jit(solution)/shard_map/ppermute | solution.py:39
  16.3 1.2 %copy-done.2 = bf16[1,1,32,128,128]{4,3,2,1,0:T(8,128)(2,1)S(1)} copy-done((bf16[1,1,32,128,128]{4,3,2,1,0:T(8,128)(2,1)S(1)}, bf16[1,1,32,128,128]{4,3,2,1,0:T(8,128)(2,1)}, u32[]{:S(2)}) %copy-start.2) | copy-done | bytes 1048600
  17.6 1.1 %shard_map.63 = (f32[8,80,128]{2,1,0:T(8,128)S(1)}, f32[32,80,128]{2,1,0:T(8,128)S(1)}, bf16[528,128]{1,0:T(8,128)(2,1)S(1)}, bf16[528,128]{1,0:T(8,128)(2,1)S(1)}, bf16[528,128]{1,0:T(8,128)(2,1)S(1)}) custom-call(s32[3,32]{1,0:T(4,128)S(1)} %shard_map.59.refs_0_.refs_1_, ...), custom_call_target="tpu_custom_call", output_to_operand_aliasing={{1}: (10, {})} | custom-call | flops 67108864 | bytes 3408256 | tf_op jit(solution)/shard_map/pallas_call | solution.py:25
  18.8 1.5 %shard_map.64 = (f32[64,80,128]{2,1,0:T(8,128)S(1)}, bf16[4,528,128]{2,1,0:T(8,128)(2,1)S(1)}) custom-call(f32[8,80,128]{2,1,0:T(8,128)S(1)} %get-tuple-element.39.refs_0_.refs_3_, s32[3,32]{1,0:T(4,128)S(1)} %shard_map.59.refs_0_.refs_1_, bf16[32,128,128]{2,1,0:T(8,128)(2,1)S(1)} %shard_map.60.refs_1_.refs_2_, ...), custom_call_target="tpu_custom_call", output_to_operand_aliasing={{0}: (7, {})} | custom-call | flops 67108864 | bytes 4194688 | tf_op jit(solution)/shard_map/pallas_call | solution.py:25
  20.9 2.7 %collective-permute-start.15 = (bf16[528,128]{1,0:T(8,128)(2,1)S(1)}, bf16[528,128]{1,0:T(8,128)(2,1)S(1)}, u32[]{:S(2)}, u32[]{:S(2)}) collective-permute-start(bf16[528,128]{1,0:T(8,128)(2,1)S(1)} %get-tuple-element.51), channel_id=1, source_target_pairs={{0,16},{8,24},{16,0},{24,8},{1,17},{9,25},{17,1},{25,9},{2,18},{10... | collective-permute-start | bytes 405512 | tf_op jit(solution)/shard_map/ppermute | solution.py:39
  23.6 1.2 %collective-permute-start.16 = (bf16[528,128]{1,0:T(8,128)(2,1)S(1)}, bf16[528,128]{1,0:T(8,128)(2,1)S(1)}, u32[]{:S(2)}, u32[]{:S(2)}) collective-permute-start(bf16[528,128]{1,0:T(8,128)(2,1)S(1)} %get-tuple-element.52), channel_id=1, source_target_pairs={{0,24},{8,16},{16,8},{24,0},{1,25},{9,17},{17,9},{25,1},{2,26},{10... | collective-permute-start | bytes 405512 | tf_op jit(solution)/shard_map/ppermute | solution.py:39
  24.9 1.8 %collective-permute-start.11 = (bf16[528,128]{1,0:T(8,128)(2,1)S(1)}, bf16[528,128]{1,0:T(8,128)(2,1)S(1)}, u32[]{:S(2)}, u32[]{:S(2)}) collective-permute-start(bf16[528,128]{1,0:T(8,128)(2,1)S(1)} %get-tuple-element.47), channel_id=1, source_target_pairs={{0,6},{1,7},{2,4},{3,5},{4,2},{5,3},{6,0},{7,1},{8,14},{9,15},{10,... | collective-permute-start | bytes 405512 | tf_op jit(solution)/shard_map/ppermute | solution.py:39
  26.7 1.2 %collective-permute-start.12 = (bf16[528,128]{1,0:T(8,128)(2,1)S(1)}, bf16[528,128]{1,0:T(8,128)(2,1)S(1)}, u32[]{:S(2)}, u32[]{:S(2)}) collective-permute-start(bf16[528,128]{1,0:T(8,128)(2,1)S(1)} %get-tuple-element.48), channel_id=1, source_target_pairs={{0,4},{1,5},{2,6},{3,7},{4,0},{5,1},{6,2},{7,3},{8,12},{9,13},{10,... | collective-permute-start | bytes 405512 | tf_op jit(solution)/shard_map/ppermute | solution.py:39
  28.0 0.8 collective-permute-done.14.refs_7_
  28.8 1.5 %collective-permute-start.13 = (bf16[528,128]{1,0:T(8,128)(2,1)S(1)}, bf16[528,128]{1,0:T(8,128)(2,1)S(1)}, u32[]{:S(2)}, u32[]{:S(2)}) collective-permute-start(bf16[528,128]{1,0:T(8,128)(2,1)S(1)} %get-tuple-element.49), channel_id=1, source_target_pairs={{0,2},{1,3},{2,0},{3,1},{4,6},{5,7},{6,4},{7,5},{8,10},{9,11},{10,... | collective-permute-start | bytes 405512 | tf_op jit(solution)/shard_map/ppermute | solution.py:39
  30.3 3.7 %collective-permute-done.15.refs_8_ = bf16[528,128]{1,0:T(8,128)(2,1)S(1)} collective-permute-done((bf16[528,128]{1,0:T(8,128)(2,1)S(1)}, bf16[528,128]{1,0:T(8,128)(2,1)S(1)}, u32[]{:S(2)}, u32[]{:S(2)}) %collective-permute-start.15) | collective-permute-done | bytes 135200 | tf_op jit(solution)/shard_map/ppermute | solution.py:39
  34.2 3.8 %collective-permute-start.25 = (bf16[8,64,128]{2,1,0:T(8,128)(2,1)S(1)}, bf16[8,64,128]{2,1,0:T(8,128)(2,1)S(1)}, u32[]{:S(2)}, u32[]{:S(2)}) collective-permute-start(bf16[8,64,128]{2,1,0:T(8,128)(2,1)S(1)} %get-tuple-element.55.refs_2_.refs_3_), channel_id=1, source_target_pairs={{0,16},{8,24},{16,0},{24,8},{1,17},{9,25},{17,1},{25,9},{2,18},{10... | collective-permute-start | bytes 393224 | tf_op jit(solution)/shard_map/ppermute | solution.py:39
  38.1 2.5 %collective-permute-start.17 = (bf16[8,64,128]{2,1,0:T(8,128)(2,1)S(1)}, bf16[8,64,128]{2,1,0:T(8,128)(2,1)S(1)}, u32[]{:S(2)}, u32[]{:S(2)}) collective-permute-start(bf16[8,64,128]{2,1,0:T(8,128)(2,1)S(1)} %get-tuple-element.55.refs_2_.refs_3_), channel_id=1, source_target_pairs={{0,6},{1,7},{2,4},{3,5},{4,2},{5,3},{6,0},{7,1},{8,14},{9,15},{10,... | collective-permute-start | bytes 393224 | tf_op jit(solution)/shard_map/ppermute | solution.py:39
  41.9 2.1 %collective-permute-done.24.refs_5_ = bf16[7,64,128]{2,1,0:T(8,128)(2,1)S(1)} collective-permute-done((bf16[7,64,128]{2,1,0:T(8,128)(2,1)S(1)}, bf16[7,64,128]{2,1,0:T(8,128)(2,1)S(1)}, u32[]{:S(2)}, u32[]{:S(2)}) %collective-permute-start.24) | collective-permute-done | bytes 114720 | tf_op jit(solution)/shard_map/ppermute | solution.py:39
  44.0 1.4 %collective-permute-start.26 = (bf16[9,64,128]{2,1,0:T(8,128)(2,1)S(1)}, bf16[9,64,128]{2,1,0:T(8,128)(2,1)S(1)}, u32[]{:S(2)}, u32[]{:S(2)}) collective-permute-start(bf16[9,64,128]{2,1,0:T(8,128)(2,1)S(1)} %pad_maximum_fusion.1), channel_id=1, source_target_pairs={{0,8},{8,0},{16,24},{24,16},{1,9},{9,1},{17,25},{25,17},{2,10},{10... | collective-permute-start | bytes 442376 | tf_op jit(solution)/shard_map/ppermute | solution.py:39
  46.9 0.8 collective-permute-done.22.refs_8_
  47.9 1.0 %shard_map.68 = (f32[8,64,128]{2,1,0:T(8,128)S(1)}, f32[32,64,128]{2,1,0:T(8,128)S(1)}, bf16[512,128]{1,0:T(8,128)(2,1)S(1)}, bf16[512,128]{1,0:T(8,128)(2,1)S(1)}, bf16[512,128]{1,0:T(8,128)(2,1)S(1)}) custom-call(s32[3,32]{1,0:T(4,128)S(1)} %shard_map.59.refs_0_.refs_1_, ...), custom_call_target="tpu_custom_call", output_to_operand_aliasing={{1}: (10, {})} | custom-call | flops 67108864 | bytes 3146112 | tf_op jit(solution)/shard_map/pallas_call | solution.py:25
  49.2 1.4 %shard_map.69 = (f32[64,64,128]{2,1,0:T(8,128)S(1)}, bf16[4,512,128]{2,1,0:T(8,128)(2,1)S(1)}) custom-call(f32[8,64,128]{2,1,0:T(8,128)S(1)} %get-tuple-element.57.refs_0_.refs_4_, s32[3,32]{1,0:T(4,128)S(1)} %shard_map.59.refs_0_.refs_1_, bf16[32,128,128]{2,1,0:T(8,128)(2,1)S(1)} %shard_map.60.refs_1_.refs_2_, ...), custom_call_target="tpu_custom_call", output_to_operand_aliasing={{0}: (7, {})} | custom-call | flops 67108864 | bytes 3670400 | tf_op jit(solution)/shard_map/pallas_call | solution.py:25
  50.8 1.7 %collective-permute-start.31 = (bf16[512,128]{1,0:T(8,128)(2,1)S(1)}, bf16[512,128]{1,0:T(8,128)(2,1)S(1)}, u32[]{:S(2)}, u32[]{:S(2)}) collective-permute-start(bf16[512,128]{1,0:T(8,128)(2,1)S(1)} %get-tuple-element.67), channel_id=1, source_target_pairs={{0,8},{8,0},{16,24},{24,16},{1,9},{9,1},{17,25},{25,17},{2,10},{10... | collective-permute-start | bytes 393224 | tf_op jit(solution)/shard_map/ppermute | solution.py:39
  52.5 0.8 collective-permute-start.32
  53.3 1.9 %collective-permute-start.33 = (bf16[512,128]{1,0:T(8,128)(2,1)S(1)}, bf16[512,128]{1,0:T(8,128)(2,1)S(1)}, u32[]{:S(2)}, u32[]{:S(2)}) collective-permute-start(bf16[512,128]{1,0:T(8,128)(2,1)S(1)} %get-tuple-element.69), channel_id=1, source_target_pairs={{0,24},{8,16},{16,8},{24,0},{1,25},{9,17},{17,9},{25,1},{2,26},{10... | collective-permute-start | bytes 393224 | tf_op jit(solution)/shard_map/ppermute | solution.py:39
  55.3 2.5 %collective-permute-start.28 = (bf16[512,128]{1,0:T(8,128)(2,1)S(1)}, bf16[512,128]{1,0:T(8,128)(2,1)S(1)}, u32[]{:S(2)}, u32[]{:S(2)}) collective-permute-start(bf16[512,128]{1,0:T(8,128)(2,1)S(1)} %get-tuple-element.64), channel_id=1, source_target_pairs={{0,6},{1,7},{2,4},{3,5},{4,2},{5,3},{6,0},{7,1},{8,14},{9,15},{10,... | collective-permute-start | bytes 393224 | tf_op jit(solution)/shard_map/ppermute | solution.py:39
  58.3 1.6 %collective-permute-start.30 = (bf16[512,128]{1,0:T(8,128)(2,1)S(1)}, bf16[512,128]{1,0:T(8,128)(2,1)S(1)}, u32[]{:S(2)}, u32[]{:S(2)}) collective-permute-start(bf16[512,128]{1,0:T(8,128)(2,1)S(1)} %get-tuple-element.66), channel_id=1, source_target_pairs={{0,2},{1,3},{2,0},{3,1},{4,6},{5,7},{6,4},{7,5},{8,10},{9,11},{10,... | collective-permute-start | bytes 393224 | tf_op jit(solution)/shard_map/ppermute | solution.py:39
  60.0 5.4 %collective-permute-done.32.refs_9_ = bf16[512,128]{1,0:T(8,128)(2,1)S(1)} collective-permute-done((bf16[512,128]{1,0:T(8,128)(2,1)S(1)}, bf16[512,128]{1,0:T(8,128)(2,1)S(1)}, u32[]{:S(2)}, u32[]{:S(2)}) %collective-permute-start.32) | collective-permute-done | bytes 131104 | tf_op jit(solution)/shard_map/ppermute | solution.py:39
  65.6 2.6 %collective-permute-start.42 = (bf16[8,64,128]{2,1,0:T(8,128)(2,1)S(1)}, bf16[8,64,128]{2,1,0:T(8,128)(2,1)S(1)}, u32[]{:S(2)}, u32[]{:S(2)}) collective-permute-start(bf16[8,64,128]{2,1,0:T(8,128)(2,1)S(1)} %get-tuple-element.71.refs_2_.refs_3_), channel_id=1, source_target_pairs={{0,16},{8,24},{16,0},{24,8},{1,17},{9,25},{17,1},{25,9},{2,18},{10... | collective-permute-start | bytes 393224 | tf_op jit(solution)/shard_map/ppermute | solution.py:39
  68.3 2.5 %collective-permute-start.34 = (bf16[8,64,128]{2,1,0:T(8,128)(2,1)S(1)}, bf16[8,64,128]{2,1,0:T(8,128)(2,1)S(1)}, u32[]{:S(2)}, u32[]{:S(2)}) collective-permute-start(bf16[8,64,128]{2,1,0:T(8,128)(2,1)S(1)} %get-tuple-element.71.refs_2_.refs_3_), channel_id=1, source_target_pairs={{0,6},{1,7},{2,4},{3,5},{4,2},{5,3},{6,0},{7,1},{8,14},{9,15},{10,... | collective-permute-start | bytes 393224 | tf_op jit(solution)/shard_map/ppermute | solution.py:39
  72.5 1.4 %collective-permute-done.41.refs_5_ = bf16[7,64,128]{2,1,0:T(8,128)(2,1)S(1)} collective-permute-done((bf16[7,64,128]{2,1,0:T(8,128)(2,1)S(1)}, bf16[7,64,128]{2,1,0:T(8,128)(2,1)S(1)}, u32[]{:S(2)}, u32[]{:S(2)}) %collective-permute-start.41) | collective-permute-done | bytes 114720 | tf_op jit(solution)/shard_map/ppermute | solution.py:39
  74.3 1.0 collective-permute-start.43
  76.9 0.8 collective-permute-done.39.refs_8_
  77.9 1.0 shard_map.72.refs_1_
  79.5 1.2 %shard_map.74 = f32[40,128]{1,0:T(8,128)S(1)} custom-call(s32[3,32]{1,0:T(4,128)S(1)} %shard_map.59.refs_0_.refs_1_, bf16[64,4096]{1,0:T(8,128)(2,1)S(1)} %shard_map.72.refs_1_, f32[64,128]{1,0:T(8,128)S(1)} %shard_map.73.refs_2_, bf16[8,64,128]{2,1,0:T(8,128)(2,1)S(1)} %get-tuple-element.71.refs_2_.refs_3_, ...), custom_call_target="tpu_custom_call" | custom-call | flops 33554432 | bytes 1081728 | tf_op jit(solution)/shard_map/pallas_call | solution.py:25
  80.8 1.2 %collective-permute-done.44 = f32[40,128]{1,0:T(8,128)S(1)} collective-permute-done((f32[40,128]{1,0:T(8,128)S(1)}, f32[40,128]{1,0:T(8,128)S(1)}, u32[]{:S(2)}, u32[]{:S(2)}) %collective-permute-start.44) | collective-permute-done | bytes 20512 | tf_op jit(solution)/shard_map/ppermute | solution.py:39
  81.9 2.0 %collective-permute-start.45 = (f32[40,128]{1,0:T(8,128)S(1)}, f32[40,128]{1,0:T(8,128)S(1)}, u32[]{:S(2)}, u32[]{:S(2)}) collective-permute-start(f32[40,128]{1,0:T(8,128)S(1)} %add.12), channel_id=1, source_target_pairs={{0,6},{1,7},{2,4},{3,5},{4,2},{5,3},{6,0},{7,1},{8,14},{9,15},{10,... | collective-permute-start | bytes 61448 | tf_op jit(solution)/shard_map/ppermute | solution.py:39
  84.0 0.9 collective-permute-start.46
  85.4 1.2 %collective-permute-done.45 = f32[40,128]{1,0:T(8,128)S(1)} collective-permute-done((f32[40,128]{1,0:T(8,128)S(1)}, f32[40,128]{1,0:T(8,128)S(1)}, u32[]{:S(2)}, u32[]{:S(2)}) %collective-permute-start.45) | collective-permute-done | bytes 20512 | tf_op jit(solution)/shard_map/ppermute | solution.py:39
  86.6 1.1 %collective-permute-done.46 = f32[40,128]{1,0:T(8,128)S(1)} collective-permute-done((f32[40,128]{1,0:T(8,128)S(1)}, f32[40,128]{1,0:T(8,128)S(1)}, u32[]{:S(2)}, u32[]{:S(2)}) %collective-permute-start.46) | collective-permute-done | bytes 20512 | tf_op jit(solution)/shard_map/ppermute | solution.py:39
  87.7 0.9 collective-permute-done.47
  88.6 1.9 %collective-permute-start.48 = (f32[40,128]{1,0:T(8,128)S(1)}, f32[40,128]{1,0:T(8,128)S(1)}, u32[]{:S(2)}, u32[]{:S(2)}) collective-permute-start(f32[40,128]{1,0:T(8,128)S(1)} %add_add_fusion.refs_1_), channel_id=1, source_target_pairs={{0,24},{8,16},{16,8},{24,0},{1,25},{9,17},{17,9},{25,1},{2,26},{10... | collective-permute-start | bytes 61448 | tf_op jit(solution)/shard_map/ppermute | solution.py:39
  90.5 0.8 collective-permute-start.49
  91.4 1.7 %collective-permute-start.50 = (f32[40,128]{1,0:T(8,128)S(1)}, f32[40,128]{1,0:T(8,128)S(1)}, u32[]{:S(2)}, u32[]{:S(2)}) collective-permute-start(f32[40,128]{1,0:T(8,128)S(1)} %add_add_fusion.refs_1_), channel_id=1, source_target_pairs={{0,8},{8,0},{16,24},{24,16},{1,9},{9,1},{17,25},{25,17},{2,10},{10... | collective-permute-start | bytes 61448 | tf_op jit(solution)/shard_map/ppermute | solution.py:39
  93.1 1.2 %collective-permute-done.48.refs_2_ = f32[40,128]{1,0:T(8,128)S(1)} collective-permute-done((f32[40,128]{1,0:T(8,128)S(1)}, f32[40,128]{1,0:T(8,128)S(1)}, u32[]{:S(2)}, u32[]{:S(2)}) %collective-permute-start.48) | collective-permute-done | bytes 20512 | tf_op jit(solution)/shard_map/ppermute | solution.py:39
  94.3 1.1 %collective-permute-done.49.refs_3_ = f32[40,128]{1,0:T(8,128)S(1)} collective-permute-done((f32[40,128]{1,0:T(8,128)S(1)}, f32[40,128]{1,0:T(8,128)S(1)}, u32[]{:S(2)}, u32[]{:S(2)}) %collective-permute-start.49) | collective-permute-done | bytes 20512 | tf_op jit(solution)/shard_map/ppermute | solution.py:39
  95.4 3.8 %shard_map.75 = (f32[64,1024]{1,0:T(8,128)}, f32[64,64]{1,0:T(8,128)}) custom-call(f32[64,1024]{1,0:T(8,128)S(1)} %get-tuple-element.70.refs_0_, f32[40,128]{1,0:T(8,128)S(1)} %add_add_fusion.refs_1_, f32[40,128]{1,0:T(8,128)S(1)} %collective-permute-done.48.refs_2_, f32[40,128]{1,0:T(8,128)S(1)} %collective-permute-done.49.refs_3_, ...), custom_call_target="tpu_custom_call" | custom-call | bytes 344064 | tf_op jit(solution)/shard_map/pallas_call | solution.py:25
  (94 shorter events, 14.4 us)
Async XLA Ops:
  1.6 11.0 %collective-permute-start.8 = (bf16[8,64,128]{2,1,0:T(8,128)(2,1)S(1)}, bf16[8,64,128]{2,1,0:T(8,128)(2,1)S(1)}, u32[]{:S(2)}, u32[]{:S(2)}) collective-permute-start(bf16[8,64,128]{2,1,0:T(8,128)(2,1)S(1)} %shard_map.61.refs_2_.refs_3_), channel_id=1, source_target_pairs={{0,16},{8,24},{16,0},{24,8},{1,17},{9,25},{17,1},{25,9},{2,18},{10... | collective-permute-start | bytes 393224 | tf_op jit(solution)/shard_map/ppermute | solution.py:39
  5.7 6.9 %collective-permute-start.7 = (bf16[7,64,128]{2,1,0:T(8,128)(2,1)S(1)}, bf16[7,64,128]{2,1,0:T(8,128)(2,1)S(1)}, u32[]{:S(2)}, u32[]{:S(2)}) collective-permute-start(bf16[7,64,128]{2,1,0:T(8,128)(2,1)S(1)} %slice.24), channel_id=1, source_target_pairs={{0,8},{8,0},{16,24},{24,16},{1,9},{9,1},{17,25},{25,17},{2,10},{10... | collective-permute-start | bytes 344072 | tf_op jit(solution)/shard_map/ppermute | solution.py:39
  7.4 6.6 %collective-permute-start = (bf16[8,64,128]{2,1,0:T(8,128)(2,1)S(1)}, bf16[8,64,128]{2,1,0:T(8,128)(2,1)S(1)}, u32[]{:S(2)}, u32[]{:S(2)}) collective-permute-start(bf16[8,64,128]{2,1,0:T(8,128)(2,1)S(1)} %shard_map.61.refs_2_.refs_3_), channel_id=1, source_target_pairs={{0,6},{1,7},{2,4},{3,5},{4,2},{5,3},{6,0},{7,1},{8,14},{9,15},{10,... | collective-permute-start | bytes 393224 | tf_op jit(solution)/shard_map/ppermute | solution.py:39
  9.8 5.9 %collective-permute-start.1 = (bf16[8,64,128]{2,1,0:T(8,128)(2,1)S(1)}, bf16[8,64,128]{2,1,0:T(8,128)(2,1)S(1)}, u32[]{:S(2)}, u32[]{:S(2)}) collective-permute-start(bf16[8,64,128]{2,1,0:T(8,128)(2,1)S(1)} %shard_map.61.refs_2_.refs_3_), channel_id=1, source_target_pairs={{0,4},{1,5},{2,6},{3,7},{4,0},{5,1},{6,2},{7,3},{8,12},{9,13},{10,... | collective-permute-start | bytes 393224 | tf_op jit(solution)/shard_map/ppermute | solution.py:39
  10.3 5.5 %collective-permute-start.2 = (bf16[8,64,128]{2,1,0:T(8,128)(2,1)S(1)}, bf16[8,64,128]{2,1,0:T(8,128)(2,1)S(1)}, u32[]{:S(2)}, u32[]{:S(2)}) collective-permute-start(bf16[8,64,128]{2,1,0:T(8,128)(2,1)S(1)} %shard_map.61.refs_2_.refs_3_), channel_id=1, source_target_pairs={{0,2},{1,3},{2,0},{3,1},{4,6},{5,7},{6,4},{7,5},{8,10},{9,11},{10,... | collective-permute-start | bytes 393224 | tf_op jit(solution)/shard_map/ppermute | solution.py:39
  12.6 6.1 %collective-permute-start.9 = (bf16[9,64,128]{2,1,0:T(8,128)(2,1)S(1)}, bf16[9,64,128]{2,1,0:T(8,128)(2,1)S(1)}, u32[]{:S(2)}, u32[]{:S(2)}) collective-permute-start(bf16[9,64,128]{2,1,0:T(8,128)(2,1)S(1)} %pad_maximum_fusion), channel_id=1, source_target_pairs={{0,8},{8,0},{16,24},{24,16},{1,9},{9,1},{17,25},{25,17},{2,10},{10... | collective-permute-start | bytes 442376 | tf_op jit(solution)/shard_map/ppermute | solution.py:39
  13.5 4.1 %collective-permute-start.3 = (bf16[8,64,128]{2,1,0:T(8,128)(2,1)S(1)}, bf16[8,64,128]{2,1,0:T(8,128)(2,1)S(1)}, u32[]{:S(2)}, u32[]{:S(2)}) collective-permute-start(bf16[8,64,128]{2,1,0:T(8,128)(2,1)S(1)} %shard_map.61.refs_2_.refs_3_), channel_id=1, source_target_pairs={{0,1},{1,0},{2,3},{3,2},{4,5},{5,4},{6,7},{7,6},{8,9},{9,8},{10,11... | collective-permute-start | bytes 393224 | tf_op jit(solution)/shard_map/ppermute | solution.py:39
  13.9 3.7 %collective-permute-start.4 = (bf16[8,64,128]{2,1,0:T(8,128)(2,1)S(1)}, bf16[8,64,128]{2,1,0:T(8,128)(2,1)S(1)}, u32[]{:S(2)}, u32[]{:S(2)}) collective-permute-start(bf16[8,64,128]{2,1,0:T(8,128)(2,1)S(1)} %collective-permute-done.refs_3_), channel_id=1, source_target_pairs={{0,1},{1,0},{2,3},{3,2},{4,5},{5,4},{6,7},{7,6},{8,9},{9,8},{10,11... | collective-permute-start | bytes 393224 | tf_op jit(solution)/shard_map/ppermute | solution.py:39
  15.7 1.8 %collective-permute-start.5 = (bf16[8,64,128]{2,1,0:T(8,128)(2,1)S(1)}, bf16[8,64,128]{2,1,0:T(8,128)(2,1)S(1)}, u32[]{:S(2)}, u32[]{:S(2)}) collective-permute-start(bf16[8,64,128]{2,1,0:T(8,128)(2,1)S(1)} %collective-permute-done.1.refs_4_), channel_id=1, source_target_pairs={{0,1},{1,0},{2,3},{3,2},{4,5},{5,4},{6,7},{7,6},{8,9},{9,8},{10,11... | collective-permute-start | bytes 393224 | tf_op jit(solution)/shard_map/ppermute | solution.py:39
  15.8 1.8 %collective-permute-start.6 = (bf16[8,64,128]{2,1,0:T(8,128)(2,1)S(1)}, bf16[8,64,128]{2,1,0:T(8,128)(2,1)S(1)}, u32[]{:S(2)}, u32[]{:S(2)}) collective-permute-start(bf16[8,64,128]{2,1,0:T(8,128)(2,1)S(1)} %collective-permute-done.2.refs_5_), channel_id=1, source_target_pairs={{0,1},{1,0},{2,3},{3,2},{4,5},{5,4},{6,7},{7,6},{8,9},{9,8},{10,11... | collective-permute-start | bytes 393224 | tf_op jit(solution)/shard_map/ppermute | solution.py:39
  20.3 4.5 %collective-permute-start.10 = (bf16[4,528,128]{2,1,0:T(8,128)(2,1)S(1)}, bf16[4,528,128]{2,1,0:T(8,128)(2,1)S(1)}, u32[]{:S(2)}, u32[]{:S(2)}) collective-permute-start(bf16[4,528,128]{2,1,0:T(8,128)(2,1)S(1)} %get-tuple-element.44), channel_id=1, source_target_pairs={{0,1},{1,0},{2,3},{3,2},{4,5},{5,4},{6,7},{7,6},{8,9},{9,8},{10,11... | collective-permute-start | bytes 1622024 | tf_op jit(solution)/shard_map/ppermute | solution.py:39
  20.4 8.4 %collective-permute-start.14 = (bf16[528,128]{1,0:T(8,128)(2,1)S(1)}, bf16[528,128]{1,0:T(8,128)(2,1)S(1)}, u32[]{:S(2)}, u32[]{:S(2)}) collective-permute-start(bf16[528,128]{1,0:T(8,128)(2,1)S(1)} %get-tuple-element.50), channel_id=1, source_target_pairs={{0,8},{8,0},{16,24},{24,16},{1,9},{9,1},{17,25},{25,17},{2,10},{10... | collective-permute-start | bytes 405512 | tf_op jit(solution)/shard_map/ppermute | solution.py:39
  20.9 13.2 %collective-permute-start.15 = (bf16[528,128]{1,0:T(8,128)(2,1)S(1)}, bf16[528,128]{1,0:T(8,128)(2,1)S(1)}, u32[]{:S(2)}, u32[]{:S(2)}) collective-permute-start(bf16[528,128]{1,0:T(8,128)(2,1)S(1)} %get-tuple-element.51), channel_id=1, source_target_pairs={{0,16},{8,24},{16,0},{24,8},{1,17},{9,25},{17,1},{25,9},{2,18},{10... | collective-permute-start | bytes 405512 | tf_op jit(solution)/shard_map/ppermute | solution.py:39
  23.6 10.4 %collective-permute-start.16 = (bf16[528,128]{1,0:T(8,128)(2,1)S(1)}, bf16[528,128]{1,0:T(8,128)(2,1)S(1)}, u32[]{:S(2)}, u32[]{:S(2)}) collective-permute-start(bf16[528,128]{1,0:T(8,128)(2,1)S(1)} %get-tuple-element.52), channel_id=1, source_target_pairs={{0,24},{8,16},{16,8},{24,0},{1,25},{9,17},{17,9},{25,1},{2,26},{10... | collective-permute-start | bytes 405512 | tf_op jit(solution)/shard_map/ppermute | solution.py:39
  24.9 9.1 %collective-permute-start.11 = (bf16[528,128]{1,0:T(8,128)(2,1)S(1)}, bf16[528,128]{1,0:T(8,128)(2,1)S(1)}, u32[]{:S(2)}, u32[]{:S(2)}) collective-permute-start(bf16[528,128]{1,0:T(8,128)(2,1)S(1)} %get-tuple-element.47), channel_id=1, source_target_pairs={{0,6},{1,7},{2,4},{3,5},{4,2},{5,3},{6,0},{7,1},{8,14},{9,15},{10,... | collective-permute-start | bytes 405512 | tf_op jit(solution)/shard_map/ppermute | solution.py:39
  26.7 7.3 %collective-permute-start.12 = (bf16[528,128]{1,0:T(8,128)(2,1)S(1)}, bf16[528,128]{1,0:T(8,128)(2,1)S(1)}, u32[]{:S(2)}, u32[]{:S(2)}) collective-permute-start(bf16[528,128]{1,0:T(8,128)(2,1)S(1)} %get-tuple-element.48), channel_id=1, source_target_pairs={{0,4},{1,5},{2,6},{3,7},{4,0},{5,1},{6,2},{7,3},{8,12},{9,13},{10,... | collective-permute-start | bytes 405512 | tf_op jit(solution)/shard_map/ppermute | solution.py:39
  28.8 5.2 %collective-permute-start.13 = (bf16[528,128]{1,0:T(8,128)(2,1)S(1)}, bf16[528,128]{1,0:T(8,128)(2,1)S(1)}, u32[]{:S(2)}, u32[]{:S(2)}) collective-permute-start(bf16[528,128]{1,0:T(8,128)(2,1)S(1)} %get-tuple-element.49), channel_id=1, source_target_pairs={{0,2},{1,3},{2,0},{3,1},{4,6},{5,7},{6,4},{7,5},{8,10},{9,11},{10,... | collective-permute-start | bytes 405512 | tf_op jit(solution)/shard_map/ppermute | solution.py:39
  34.2 9.7 %collective-permute-start.25 = (bf16[8,64,128]{2,1,0:T(8,128)(2,1)S(1)}, bf16[8,64,128]{2,1,0:T(8,128)(2,1)S(1)}, u32[]{:S(2)}, u32[]{:S(2)}) collective-permute-start(bf16[8,64,128]{2,1,0:T(8,128)(2,1)S(1)} %get-tuple-element.55.refs_2_.refs_3_), channel_id=1, source_target_pairs={{0,16},{8,24},{16,0},{24,8},{1,17},{9,25},{17,1},{25,9},{2,18},{10... | collective-permute-start | bytes 393224 | tf_op jit(solution)/shard_map/ppermute | solution.py:39
  38.0 5.9 %collective-permute-start.24 = (bf16[7,64,128]{2,1,0:T(8,128)(2,1)S(1)}, bf16[7,64,128]{2,1,0:T(8,128)(2,1)S(1)}, u32[]{:S(2)}, u32[]{:S(2)}) collective-permute-start(bf16[7,64,128]{2,1,0:T(8,128)(2,1)S(1)} %slice.20), channel_id=1, source_target_pairs={{0,8},{8,0},{16,24},{24,16},{1,9},{9,1},{17,25},{25,17},{2,10},{10... | collective-permute-start | bytes 344072 | tf_op jit(solution)/shard_map/ppermute | solution.py:39
  38.1 7.2 %collective-permute-start.17 = (bf16[8,64,128]{2,1,0:T(8,128)(2,1)S(1)}, bf16[8,64,128]{2,1,0:T(8,128)(2,1)S(1)}, u32[]{:S(2)}, u32[]{:S(2)}) collective-permute-start(bf16[8,64,128]{2,1,0:T(8,128)(2,1)S(1)} %get-tuple-element.55.refs_2_.refs_3_), channel_id=1, source_target_pairs={{0,6},{1,7},{2,4},{3,5},{4,2},{5,3},{6,0},{7,1},{8,14},{9,15},{10,... | collective-permute-start | bytes 393224 | tf_op jit(solution)/shard_map/ppermute | solution.py:39
  40.6 5.7 %collective-permute-start.18 = (bf16[8,64,128]{2,1,0:T(8,128)(2,1)S(1)}, bf16[8,64,128]{2,1,0:T(8,128)(2,1)S(1)}, u32[]{:S(2)}, u32[]{:S(2)}) collective-permute-start(bf16[8,64,128]{2,1,0:T(8,128)(2,1)S(1)} %get-tuple-element.55.refs_2_.refs_3_), channel_id=1, source_target_pairs={{0,4},{1,5},{2,6},{3,7},{4,0},{5,1},{6,2},{7,3},{8,12},{9,13},{10,... | collective-permute-start | bytes 393224 | tf_op jit(solution)/shard_map/ppermute | solution.py:39
  41.1 5.3 %collective-permute-start.19 = (bf16[8,64,128]{2,1,0:T(8,128)(2,1)S(1)}, bf16[8,64,128]{2,1,0:T(8,128)(2,1)S(1)}, u32[]{:S(2)}, u32[]{:S(2)}) collective-permute-start(bf16[8,64,128]{2,1,0:T(8,128)(2,1)S(1)} %get-tuple-element.55.refs_2_.refs_3_), channel_id=1, source_target_pairs={{0,2},{1,3},{2,0},{3,1},{4,6},{5,7},{6,4},{7,5},{8,10},{9,11},{10,... | collective-permute-start | bytes 393224 | tf_op jit(solution)/shard_map/ppermute | solution.py:39
  44.0 5.2 %collective-permute-start.26 = (bf16[9,64,128]{2,1,0:T(8,128)(2,1)S(1)}, bf16[9,64,128]{2,1,0:T(8,128)(2,1)S(1)}, u32[]{:S(2)}, u32[]{:S(2)}) collective-permute-start(bf16[9,64,128]{2,1,0:T(8,128)(2,1)S(1)} %pad_maximum_fusion.1), channel_id=1, source_target_pairs={{0,8},{8,0},{16,24},{24,16},{1,9},{9,1},{17,25},{25,17},{2,10},{10... | collective-permute-start | bytes 442376 | tf_op jit(solution)/shard_map/ppermute | solution.py:39
  45.3 1.5 %collective-permute-start.20 = (bf16[8,64,128]{2,1,0:T(8,128)(2,1)S(1)}, bf16[8,64,128]{2,1,0:T(8,128)(2,1)S(1)}, u32[]{:S(2)}, u32[]{:S(2)}) collective-permute-start(bf16[8,64,128]{2,1,0:T(8,128)(2,1)S(1)} %get-tuple-element.55.refs_2_.refs_3_), channel_id=1, source_target_pairs={{0,1},{1,0},{2,3},{3,2},{4,5},{5,4},{6,7},{7,6},{8,9},{9,8},{10,11... | collective-permute-start | bytes 393224 | tf_op jit(solution)/shard_map/ppermute | solution.py:39
  45.3 1.5 %collective-permute-start.21 = (bf16[8,64,128]{2,1,0:T(8,128)(2,1)S(1)}, bf16[8,64,128]{2,1,0:T(8,128)(2,1)S(1)}, u32[]{:S(2)}, u32[]{:S(2)}) collective-permute-start(bf16[8,64,128]{2,1,0:T(8,128)(2,1)S(1)} %collective-permute-done.17.refs_3_), channel_id=1, source_target_pairs={{0,1},{1,0},{2,3},{3,2},{4,5},{5,4},{6,7},{7,6},{8,9},{9,8},{10,11... | collective-permute-start | bytes 393224 | tf_op jit(solution)/shard_map/ppermute | solution.py:39
  46.4 1.4 %collective-permute-start.23 = (bf16[8,64,128]{2,1,0:T(8,128)(2,1)S(1)}, bf16[8,64,128]{2,1,0:T(8,128)(2,1)S(1)}, u32[]{:S(2)}, u32[]{:S(2)}) collective-permute-start(bf16[8,64,128]{2,1,0:T(8,128)(2,1)S(1)} %collective-permute-done.19.refs_5_), channel_id=1, source_target_pairs={{0,1},{1,0},{2,3},{3,2},{4,5},{5,4},{6,7},{7,6},{8,9},{9,8},{10,11... | collective-permute-start | bytes 393224 | tf_op jit(solution)/shard_map/ppermute | solution.py:39
  50.6 4.6 %collective-permute-start.27 = (bf16[4,512,128]{2,1,0:T(8,128)(2,1)S(1)}, bf16[4,512,128]{2,1,0:T(8,128)(2,1)S(1)}, u32[]{:S(2)}, u32[]{:S(2)}) collective-permute-start(bf16[4,512,128]{2,1,0:T(8,128)(2,1)S(1)} %get-tuple-element.62), channel_id=1, source_target_pairs={{0,1},{1,0},{2,3},{3,2},{4,5},{5,4},{6,7},{7,6},{8,9},{9,8},{10,11... | collective-permute-start | bytes 1572872 | tf_op jit(solution)/shard_map/ppermute | solution.py:39
  50.8 7.5 %collective-permute-start.31 = (bf16[512,128]{1,0:T(8,128)(2,1)S(1)}, bf16[512,128]{1,0:T(8,128)(2,1)S(1)}, u32[]{:S(2)}, u32[]{:S(2)}) collective-permute-start(bf16[512,128]{1,0:T(8,128)(2,1)S(1)} %get-tuple-element.67), channel_id=1, source_target_pairs={{0,8},{8,0},{16,24},{24,16},{1,9},{9,1},{17,25},{25,17},{2,10},{10... | collective-permute-start | bytes 393224 | tf_op jit(solution)/shard_map/ppermute | solution.py:39
  52.5 12.9 %collective-permute-start.32 = (bf16[512,128]{1,0:T(8,128)(2,1)S(1)}, bf16[512,128]{1,0:T(8,128)(2,1)S(1)}, u32[]{:S(2)}, u32[]{:S(2)}) collective-permute-start(bf16[512,128]{1,0:T(8,128)(2,1)S(1)} %get-tuple-element.68), channel_id=1, source_target_pairs={{0,16},{8,24},{16,0},{24,8},{1,17},{9,25},{17,1},{25,9},{2,18},{10... | collective-permute-start | bytes 393224 | tf_op jit(solution)/shard_map/ppermute | solution.py:39
  53.3 12.1 %collective-permute-start.33 = (bf16[512,128]{1,0:T(8,128)(2,1)S(1)}, bf16[512,128]{1,0:T(8,128)(2,1)S(1)}, u32[]{:S(2)}, u32[]{:S(2)}) collective-permute-start(bf16[512,128]{1,0:T(8,128)(2,1)S(1)} %get-tuple-element.69), channel_id=1, source_target_pairs={{0,24},{8,16},{16,8},{24,0},{1,25},{9,17},{17,9},{25,1},{2,26},{10... | collective-permute-start | bytes 393224 | tf_op jit(solution)/shard_map/ppermute | solution.py:39
  55.3 10.1 %collective-permute-start.28 = (bf16[512,128]{1,0:T(8,128)(2,1)S(1)}, bf16[512,128]{1,0:T(8,128)(2,1)S(1)}, u32[]{:S(2)}, u32[]{:S(2)}) collective-permute-start(bf16[512,128]{1,0:T(8,128)(2,1)S(1)} %get-tuple-element.64), channel_id=1, source_target_pairs={{0,6},{1,7},{2,4},{3,5},{4,2},{5,3},{6,0},{7,1},{8,14},{9,15},{10,... | collective-permute-start | bytes 393224 | tf_op jit(solution)/shard_map/ppermute | solution.py:39
  57.8 7.6 %collective-permute-start.29 = (bf16[512,128]{1,0:T(8,128)(2,1)S(1)}, bf16[512,128]{1,0:T(8,128)(2,1)S(1)}, u32[]{:S(2)}, u32[]{:S(2)}) collective-permute-start(bf16[512,128]{1,0:T(8,128)(2,1)S(1)} %get-tuple-element.65), channel_id=1, source_target_pairs={{0,4},{1,5},{2,6},{3,7},{4,0},{5,1},{6,2},{7,3},{8,12},{9,13},{10,... | collective-permute-start | bytes 393224 | tf_op jit(solution)/shard_map/ppermute | solution.py:39
  58.3 7.1 %collective-permute-start.30 = (bf16[512,128]{1,0:T(8,128)(2,1)S(1)}, bf16[512,128]{1,0:T(8,128)(2,1)S(1)}, u32[]{:S(2)}, u32[]{:S(2)}) collective-permute-start(bf16[512,128]{1,0:T(8,128)(2,1)S(1)} %get-tuple-element.66), channel_id=1, source_target_pairs={{0,2},{1,3},{2,0},{3,1},{4,6},{5,7},{6,4},{7,5},{8,10},{9,11},{10,... | collective-permute-start | bytes 393224 | tf_op jit(solution)/shard_map/ppermute | solution.py:39
  65.6 8.7 %collective-permute-start.42 = (bf16[8,64,128]{2,1,0:T(8,128)(2,1)S(1)}, bf16[8,64,128]{2,1,0:T(8,128)(2,1)S(1)}, u32[]{:S(2)}, u32[]{:S(2)}) collective-permute-start(bf16[8,64,128]{2,1,0:T(8,128)(2,1)S(1)} %get-tuple-element.71.refs_2_.refs_3_), channel_id=1, source_target_pairs={{0,16},{8,24},{16,0},{24,8},{1,17},{9,25},{17,1},{25,9},{2,18},{10... | collective-permute-start | bytes 393224 | tf_op jit(solution)/shard_map/ppermute | solution.py:39
  68.2 5.7 %collective-permute-start.41 = (bf16[7,64,128]{2,1,0:T(8,128)(2,1)S(1)}, bf16[7,64,128]{2,1,0:T(8,128)(2,1)S(1)}, u32[]{:S(2)}, u32[]{:S(2)}) collective-permute-start(bf16[7,64,128]{2,1,0:T(8,128)(2,1)S(1)} %slice.22), channel_id=1, source_target_pairs={{0,8},{8,0},{16,24},{24,16},{1,9},{9,1},{17,25},{25,17},{2,10},{10... | collective-permute-start | bytes 344072 | tf_op jit(solution)/shard_map/ppermute | solution.py:39
  68.3 7.0 %collective-permute-start.34 = (bf16[8,64,128]{2,1,0:T(8,128)(2,1)S(1)}, bf16[8,64,128]{2,1,0:T(8,128)(2,1)S(1)}, u32[]{:S(2)}, u32[]{:S(2)}) collective-permute-start(bf16[8,64,128]{2,1,0:T(8,128)(2,1)S(1)} %get-tuple-element.71.refs_2_.refs_3_), channel_id=1, source_target_pairs={{0,6},{1,7},{2,4},{3,5},{4,2},{5,3},{6,0},{7,1},{8,14},{9,15},{10,... | collective-permute-start | bytes 393224 | tf_op jit(solution)/shard_map/ppermute | solution.py:39
  70.8 5.6 %collective-permute-start.35 = (bf16[8,64,128]{2,1,0:T(8,128)(2,1)S(1)}, bf16[8,64,128]{2,1,0:T(8,128)(2,1)S(1)}, u32[]{:S(2)}, u32[]{:S(2)}) collective-permute-start(bf16[8,64,128]{2,1,0:T(8,128)(2,1)S(1)} %get-tuple-element.71.refs_2_.refs_3_), channel_id=1, source_target_pairs={{0,4},{1,5},{2,6},{3,7},{4,0},{5,1},{6,2},{7,3},{8,12},{9,13},{10,... | collective-permute-start | bytes 393224 | tf_op jit(solution)/shard_map/ppermute | solution.py:39
  71.3 5.2 %collective-permute-start.36 = (bf16[8,64,128]{2,1,0:T(8,128)(2,1)S(1)}, bf16[8,64,128]{2,1,0:T(8,128)(2,1)S(1)}, u32[]{:S(2)}, u32[]{:S(2)}) collective-permute-start(bf16[8,64,128]{2,1,0:T(8,128)(2,1)S(1)} %get-tuple-element.71.refs_2_.refs_3_), channel_id=1, source_target_pairs={{0,2},{1,3},{2,0},{3,1},{4,6},{5,7},{6,4},{7,5},{8,10},{9,11},{10,... | collective-permute-start | bytes 393224 | tf_op jit(solution)/shard_map/ppermute | solution.py:39
  74.3 5.2 %collective-permute-start.43 = (bf16[9,64,128]{2,1,0:T(8,128)(2,1)S(1)}, bf16[9,64,128]{2,1,0:T(8,128)(2,1)S(1)}, u32[]{:S(2)}, u32[]{:S(2)}) collective-permute-start(bf16[9,64,128]{2,1,0:T(8,128)(2,1)S(1)} %pad_maximum_fusion.2), channel_id=1, source_target_pairs={{0,8},{8,0},{16,24},{24,16},{1,9},{9,1},{17,25},{25,17},{2,10},{10... | collective-permute-start | bytes 442376 | tf_op jit(solution)/shard_map/ppermute | solution.py:39
  75.2 1.7 %collective-permute-start.37 = (bf16[8,64,128]{2,1,0:T(8,128)(2,1)S(1)}, bf16[8,64,128]{2,1,0:T(8,128)(2,1)S(1)}, u32[]{:S(2)}, u32[]{:S(2)}) collective-permute-start(bf16[8,64,128]{2,1,0:T(8,128)(2,1)S(1)} %get-tuple-element.71.refs_2_.refs_3_), channel_id=1, source_target_pairs={{0,1},{1,0},{2,3},{3,2},{4,5},{5,4},{6,7},{7,6},{8,9},{9,8},{10,11... | collective-permute-start | bytes 393224 | tf_op jit(solution)/shard_map/ppermute | solution.py:39
  75.2 1.7 %collective-permute-start.38 = (bf16[8,64,128]{2,1,0:T(8,128)(2,1)S(1)}, bf16[8,64,128]{2,1,0:T(8,128)(2,1)S(1)}, u32[]{:S(2)}, u32[]{:S(2)}) collective-permute-start(bf16[8,64,128]{2,1,0:T(8,128)(2,1)S(1)} %collective-permute-done.34.refs_3_), channel_id=1, source_target_pairs={{0,1},{1,0},{2,3},{3,2},{4,5},{5,4},{6,7},{7,6},{8,9},{9,8},{10,11... | collective-permute-start | bytes 393224 | tf_op jit(solution)/shard_map/ppermute | solution.py:39
  76.5 1.4 %collective-permute-start.40 = (bf16[8,64,128]{2,1,0:T(8,128)(2,1)S(1)}, bf16[8,64,128]{2,1,0:T(8,128)(2,1)S(1)}, u32[]{:S(2)}, u32[]{:S(2)}) collective-permute-start(bf16[8,64,128]{2,1,0:T(8,128)(2,1)S(1)} %collective-permute-done.36.refs_5_), channel_id=1, source_target_pairs={{0,1},{1,0},{2,3},{3,2},{4,5},{5,4},{6,7},{7,6},{8,9},{9,8},{10,11... | collective-permute-start | bytes 393224 | tf_op jit(solution)/shard_map/ppermute | solution.py:39
  81.9 4.7 %collective-permute-start.45 = (f32[40,128]{1,0:T(8,128)S(1)}, f32[40,128]{1,0:T(8,128)S(1)}, u32[]{:S(2)}, u32[]{:S(2)}) collective-permute-start(f32[40,128]{1,0:T(8,128)S(1)} %add.12), channel_id=1, source_target_pairs={{0,6},{1,7},{2,4},{3,5},{4,2},{5,3},{6,0},{7,1},{8,14},{9,15},{10,... | collective-permute-start | bytes 61448 | tf_op jit(solution)/shard_map/ppermute | solution.py:39
  84.0 3.8 %collective-permute-start.46 = (f32[40,128]{1,0:T(8,128)S(1)}, f32[40,128]{1,0:T(8,128)S(1)}, u32[]{:S(2)}, u32[]{:S(2)}) collective-permute-start(f32[40,128]{1,0:T(8,128)S(1)} %add.12), channel_id=1, source_target_pairs={{0,4},{1,5},{2,6},{3,7},{4,0},{5,1},{6,2},{7,3},{8,12},{9,13},{10,... | collective-permute-start | bytes 61448 | tf_op jit(solution)/shard_map/ppermute | solution.py:39
  84.8 3.8 %collective-permute-start.47 = (f32[40,128]{1,0:T(8,128)S(1)}, f32[40,128]{1,0:T(8,128)S(1)}, u32[]{:S(2)}, u32[]{:S(2)}) collective-permute-start(f32[40,128]{1,0:T(8,128)S(1)} %add.12), channel_id=1, source_target_pairs={{0,2},{1,3},{2,0},{3,1},{4,6},{5,7},{6,4},{7,5},{8,10},{9,11},{10,... | collective-permute-start | bytes 61448 | tf_op jit(solution)/shard_map/ppermute | solution.py:39
  88.6 5.6 %collective-permute-start.48 = (f32[40,128]{1,0:T(8,128)S(1)}, f32[40,128]{1,0:T(8,128)S(1)}, u32[]{:S(2)}, u32[]{:S(2)}) collective-permute-start(f32[40,128]{1,0:T(8,128)S(1)} %add_add_fusion.refs_1_), channel_id=1, source_target_pairs={{0,24},{8,16},{16,8},{24,0},{1,25},{9,17},{17,9},{25,1},{2,26},{10... | collective-permute-start | bytes 61448 | tf_op jit(solution)/shard_map/ppermute | solution.py:39
  90.5 4.9 %collective-permute-start.49 = (f32[40,128]{1,0:T(8,128)S(1)}, f32[40,128]{1,0:T(8,128)S(1)}, u32[]{:S(2)}, u32[]{:S(2)}) collective-permute-start(f32[40,128]{1,0:T(8,128)S(1)} %add_add_fusion.refs_1_), channel_id=1, source_target_pairs={{0,16},{8,24},{16,0},{24,8},{1,17},{9,25},{17,1},{25,9},{2,18},{10... | collective-permute-start | bytes 61448 | tf_op jit(solution)/shard_map/ppermute | solution.py:39
  91.4 4.0 %collective-permute-start.50 = (f32[40,128]{1,0:T(8,128)S(1)}, f32[40,128]{1,0:T(8,128)S(1)}, u32[]{:S(2)}, u32[]{:S(2)}) collective-permute-start(f32[40,128]{1,0:T(8,128)S(1)} %add_add_fusion.refs_1_), channel_id=1, source_target_pairs={{0,8},{8,0},{16,24},{24,16},{1,9},{9,1},{17,25},{25,17},{2,10},{10... | collective-permute-start | bytes 61448 | tf_op jit(solution)/shard_map/ppermute | solution.py:39
  (8 other events, 21.2 us)

commit v22 on v21

--- a/solution.py
+++ b/solution.py
@@ -48,30 +48,10 @@
     return [ref[:, k * width : (k + 1) * width] for k in range(ref.shape[1] // width)]
 
 
-def round_kernel(vec_ref, out_ref):
+def round_kernel(vec_ref, meta, rows_ref, cols_ref, out_ref, table):
+    group = out_ref.shape[0]
     for k, piece in enumerate(tiles_first(vec_ref, out_ref.shape[2])):
         out_ref[k] = piece.astype(BF16)
-
-
-def split_degree(sums):
-    high = sums.astype(BF16).astype(F32)
-    return jnp.concatenate([high, sums - high], 0).astype(BF16)
-
-
-def join_degree(payload, group):
-    parts = payload[payload.shape[0] - 2 * group :, :].astype(F32)
-    return parts[:group] + parts[group:]
-
-
-def fill(panel, parts, runs):
-    for part, places in zip(parts, runs):
-        at = 0
-        for place, count in places:
-            panel[place : place + count, : part.shape[1], :] = part[at : at + count]
-            at += count
-
-
-def table_kernel(group, meta, rows_ref, cols_ref, table):
     rows, cols = rows_ref[...], cols_ref[...]
     apart = lax.div(rows, group) ^ meta[1:2, :]
     halves = lax.rem(apart, 2) * meta[2:3, :] + lax.div(apart, 2)
@@ -79,6 +59,24 @@
     table[0:1, :] = (lax.div(cols, group) ^ meta[0:1, :]) * group + lax.rem(cols, group)
     table[1:2, :] = apart * group + inside
     table[2:3, :] = halves * group + inside
+
+
+def split_degree(sums):
+    high = sums.astype(BF16).astype(F32)
+    return jnp.concatenate([high, sums - high], 0).astype(BF16)
+
+
+def join_degree(payload, group):
+    parts = payload[payload.shape[0] - 2 * group :, :].astype(F32)
+    return parts[:group] + parts[group:]
+
+
+def fill(panel, parts, runs):
+    for part, places in zip(parts, runs):
+        at = 0
+        for place, count in places:
+            panel[place : place + count, : part.shape[1], :] = part[at : at + count]
+            at += count
 
 
 def fetch(source, table, arrived):
@@ -439,15 +437,14 @@
         row_got = exchange(row_send[len(row_degree) :], "col", 2)[::-1]
         return [*row_degree, row_own, col_own, *row_got, *col_got]
 
-    rounded = call(round_kernel, rounded_shape, [], 16, [start])
     meta = jnp.stack([lax.axis_index("row"), lax.axis_index("col"), chips_n]).astype(jnp.int32)
     meta = jnp.broadcast_to(meta[:, None], (3, tiles.shape[0]))
-    table = call(
-        functools.partial(table_kernel, group),
-        jax.ShapeDtypeStruct((3, tiles.shape[0]), jnp.int32),
+    rounded, table = call(
+        round_kernel,
+        [rounded_shape, jax.ShapeDtypeStruct((3, tiles.shape[0]), jnp.int32)],
         [],
         16,
-        [meta, tile_rows[None], tile_cols[None]],
+        [start, meta, tile_rows[None], tile_cols[None]],
     )
     tiles = call(
         hold_kernel,
@@ -462,7 +459,7 @@
         [vector_shape, rounded_shape, degree_shape],
         [],
         24,
-        [start, *apply(rounded, table, True, (table,))],
+        [start, *apply(rounded, table, True)],
     )
     filtered, rounded = call(
         functools.partial(filter_kernel, chips_n),

time: 99.3 us -> 101 us (1.017)
    ppermute x51, waiting for transfers between devices: 27 us -> 28 us  [trade(): return lax.ppermute(part, axis, [(i, i ^ d) for i in range(n)])]
    pallas_call x17 -> x16, Pallas kernels: 12.9 us -> 12.9 us  [call(): pl.pallas_call(lambda *refs: kernel(*refs[len(after):]), out_shape=jax.tr...]
  transfers between devices with their start and end apart: 51 -> 51, of which waited for: 25 -> 26; matrix products, arithmetic and copies ran while one was open for 0% -> 0% of each run, Pallas kernels for 5% -> 5%
where the time goes in v22:
time: 101 us
  starting transfers between devices  55.1 us (55%)
  waiting for transfers between devices  28 us (28%)
  Pallas kernels  12.9 us (13%)
  local copies, waits for them, and re-layouts  3.6 us (4%)
    ppermute x51, starting transfers between devices, trade(): return lax.ppermute(part, axis, [(i, i ^ d) for i in range(n)])  55.1 us
    ppermute x51, waiting for transfers between devices, trade(): return lax.ppermute(part, axis, [(i, i ^ d) for i in range(n)])  28 us
    pallas_call x16, Pallas kernels, call(): pl.pallas_call(lambda *refs: kernel(*refs[len(after):]), out_shape=jax.tr...  12.9 us
    unnamed x10, local copies, waits for them, and re-layouts  3.49 us
  transfers between devices with their start and end apart: 51, of which 26 were waited for; matrix products, arithmetic and copies ran while one was open for 0% of the time, Pallas kernels for 5%

profile of v22, /device:TPU:0, one launch (start us, length us, event | category | flops | bytes accessed | tf_op | source)
XLA Modules:
  0.0 100.6 jit_solution(6340320479640582364)
XLA Ops:
  0.8 0.9 copy-done
  3.1 4.1 %collective-permute-start.8 = (bf16[8,64,128]{2,1,0:T(8,128)(2,1)S(1)}, bf16[8,64,128]{2,1,0:T(8,128)(2,1)S(1)}, u32[]{:S(2)}, u32[]{:S(2)}) collective-permute-start(bf16[8,64,128]{2,1,0:T(8,128)(2,1)S(1)} %get-tuple-element.41.refs_2_.refs_3_), channel_id=1, source_target_pairs={{0,16},{8,24},{16,0},{24,8},{1,17},{9,25},{17,1},{25,9},{2,18},{10... | collective-permute-start | bytes 393224 | tf_op jit(solution)/shard_map/ppermute | solution.py:39
  7.2 1.6 %collective-permute-start.7 = (bf16[7,64,128]{2,1,0:T(8,128)(2,1)S(1)}, bf16[7,64,128]{2,1,0:T(8,128)(2,1)S(1)}, u32[]{:S(2)}, u32[]{:S(2)}) collective-permute-start(bf16[7,64,128]{2,1,0:T(8,128)(2,1)S(1)} %slice.18), channel_id=1, source_target_pairs={{0,8},{8,0},{16,24},{24,16},{1,9},{9,1},{17,25},{25,17},{2,10},{10... | collective-permute-start | bytes 344072 | tf_op jit(solution)/shard_map/ppermute | solution.py:39
  8.8 2.4 %collective-permute-start = (bf16[8,64,128]{2,1,0:T(8,128)(2,1)S(1)}, bf16[8,64,128]{2,1,0:T(8,128)(2,1)S(1)}, u32[]{:S(2)}, u32[]{:S(2)}) collective-permute-start(bf16[8,64,128]{2,1,0:T(8,128)(2,1)S(1)} %get-tuple-element.41.refs_2_.refs_3_), channel_id=1, source_target_pairs={{0,6},{1,7},{2,4},{3,5},{4,2},{5,3},{6,0},{7,1},{8,14},{9,15},{10,... | collective-permute-start | bytes 393224 | tf_op jit(solution)/shard_map/ppermute | solution.py:39
  12.6 1.1 %collective-permute-done.7.refs_5_ = bf16[7,64,128]{2,1,0:T(8,128)(2,1)S(1)} collective-permute-done((bf16[7,64,128]{2,1,0:T(8,128)(2,1)S(1)}, bf16[7,64,128]{2,1,0:T(8,128)(2,1)S(1)}, u32[]{:S(2)}, u32[]{:S(2)}) %collective-permute-start.7) | collective-permute-done | bytes 114720 | tf_op jit(solution)/shard_map/ppermute | solution.py:39
  13.7 1.3 %collective-permute-start.9 = (bf16[9,64,128]{2,1,0:T(8,128)(2,1)S(1)}, bf16[9,64,128]{2,1,0:T(8,128)(2,1)S(1)}, u32[]{:S(2)}, u32[]{:S(2)}) collective-permute-start(bf16[9,64,128]{2,1,0:T(8,128)(2,1)S(1)} %pad_maximum_fusion), channel_id=1, source_target_pairs={{0,8},{8,0},{16,24},{24,16},{1,9},{9,1},{17,25},{25,17},{2,10},{10... | collective-permute-start | bytes 442376 | tf_op jit(solution)/shard_map/ppermute | solution.py:39
  15.5 1.7 %collective-permute-done.1.refs_4_ = bf16[8,64,128]{2,1,0:T(8,128)(2,1)S(1)} collective-permute-done((bf16[8,64,128]{2,1,0:T(8,128)(2,1)S(1)}, bf16[8,64,128]{2,1,0:T(8,128)(2,1)S(1)}, u32[]{:S(2)}, u32[]{:S(2)}) %collective-permute-start.1) | collective-permute-done | bytes 131104 | tf_op jit(solution)/shard_map/ppermute | solution.py:39
  17.7 1.2 %copy-done.2 = bf16[1,1,32,128,128]{4,3,2,1,0:T(8,128)(2,1)S(1)} copy-done((bf16[1,1,32,128,128]{4,3,2,1,0:T(8,128)(2,1)S(1)}, bf16[1,1,32,128,128]{4,3,2,1,0:T(8,128)(2,1)}, u32[]{:S(2)}) %copy-start.2) | copy-done | bytes 1048600
  19.1 1.1 %shard_map.62 = (f32[8,80,128]{2,1,0:T(8,128)S(1)}, f32[32,80,128]{2,1,0:T(8,128)S(1)}, bf16[528,128]{1,0:T(8,128)(2,1)S(1)}, bf16[528,128]{1,0:T(8,128)(2,1)S(1)}, bf16[528,128]{1,0:T(8,128)(2,1)S(1)}) custom-call(s32[3,32]{1,0:T(4,128)S(1)} %get-tuple-element.40.refs_0_.refs_1_, ...), custom_call_target="tpu_custom_call", output_to_operand_aliasing={{1}: (10, {})} | custom-call | flops 67108864 | bytes 3408256 | tf_op jit(solution)/shard_map/pallas_call | solution.py:25
  20.2 1.5 %shard_map.63 = (f32[64,80,128]{2,1,0:T(8,128)S(1)}, bf16[4,528,128]{2,1,0:T(8,128)(2,1)S(1)}) custom-call(f32[8,80,128]{2,1,0:T(8,128)S(1)} %get-tuple-element.43.refs_0_.refs_3_, s32[3,32]{1,0:T(4,128)S(1)} %get-tuple-element.40.refs_0_.refs_1_, bf16[32,128,128]{2,1,0:T(8,128)(2,1)S(1)} %shard_map.60.refs_1_.refs_2_, ...), custom_call_target="tpu_custom_call", output_to_operand_aliasing={{0}: (7, {})} | custom-call | flops 67108864 | bytes 4194688 | tf_op jit(solution)/shard_map/pallas_call | solution.py:25
  22.4 2.7 %collective-permute-start.15 = (bf16[528,128]{1,0:T(8,128)(2,1)S(1)}, bf16[528,128]{1,0:T(8,128)(2,1)S(1)}, u32[]{:S(2)}, u32[]{:S(2)}) collective-permute-start(bf16[528,128]{1,0:T(8,128)(2,1)S(1)} %get-tuple-element.55), channel_id=1, source_target_pairs={{0,16},{8,24},{16,0},{24,8},{1,17},{9,25},{17,1},{25,9},{2,18},{10... | collective-permute-start | bytes 405512 | tf_op jit(solution)/shard_map/ppermute | solution.py:39
  25.1 1.2 %collective-permute-start.16 = (bf16[528,128]{1,0:T(8,128)(2,1)S(1)}, bf16[528,128]{1,0:T(8,128)(2,1)S(1)}, u32[]{:S(2)}, u32[]{:S(2)}) collective-permute-start(bf16[528,128]{1,0:T(8,128)(2,1)S(1)} %get-tuple-element.56), channel_id=1, source_target_pairs={{0,24},{8,16},{16,8},{24,0},{1,25},{9,17},{17,9},{25,1},{2,26},{10... | collective-permute-start | bytes 405512 | tf_op jit(solution)/shard_map/ppermute | solution.py:39
  26.4 1.8 %collective-permute-start.11 = (bf16[528,128]{1,0:T(8,128)(2,1)S(1)}, bf16[528,128]{1,0:T(8,128)(2,1)S(1)}, u32[]{:S(2)}, u32[]{:S(2)}) collective-permute-start(bf16[528,128]{1,0:T(8,128)(2,1)S(1)} %get-tuple-element.51), channel_id=1, source_target_pairs={{0,6},{1,7},{2,4},{3,5},{4,2},{5,3},{6,0},{7,1},{8,14},{9,15},{10,... | collective-permute-start | bytes 405512 | tf_op jit(solution)/shard_map/ppermute | solution.py:39
  28.2 1.2 %collective-permute-start.12 = (bf16[528,128]{1,0:T(8,128)(2,1)S(1)}, bf16[528,128]{1,0:T(8,128)(2,1)S(1)}, u32[]{:S(2)}, u32[]{:S(2)}) collective-permute-start(bf16[528,128]{1,0:T(8,128)(2,1)S(1)} %get-tuple-element.52), channel_id=1, source_target_pairs={{0,4},{1,5},{2,6},{3,7},{4,0},{5,1},{6,2},{7,3},{8,12},{9,13},{10,... | collective-permute-start | bytes 405512 | tf_op jit(solution)/shard_map/ppermute | solution.py:39
  29.5 0.8 collective-permute-done.14.refs_7_
  30.3 1.5 %collective-permute-start.13 = (bf16[528,128]{1,0:T(8,128)(2,1)S(1)}, bf16[528,128]{1,0:T(8,128)(2,1)S(1)}, u32[]{:S(2)}, u32[]{:S(2)}) collective-permute-start(bf16[528,128]{1,0:T(8,128)(2,1)S(1)} %get-tuple-element.53), channel_id=1, source_target_pairs={{0,2},{1,3},{2,0},{3,1},{4,6},{5,7},{6,4},{7,5},{8,10},{9,11},{10,... | collective-permute-start | bytes 405512 | tf_op jit(solution)/shard_map/ppermute | solution.py:39
  31.8 3.7 %collective-permute-done.15.refs_8_ = bf16[528,128]{1,0:T(8,128)(2,1)S(1)} collective-permute-done((bf16[528,128]{1,0:T(8,128)(2,1)S(1)}, bf16[528,128]{1,0:T(8,128)(2,1)S(1)}, u32[]{:S(2)}, u32[]{:S(2)}) %collective-permute-start.15) | collective-permute-done | bytes 135200 | tf_op jit(solution)/shard_map/ppermute | solution.py:39
  35.7 3.7 %collective-permute-start.25 = (bf16[8,64,128]{2,1,0:T(8,128)(2,1)S(1)}, bf16[8,64,128]{2,1,0:T(8,128)(2,1)S(1)}, u32[]{:S(2)}, u32[]{:S(2)}) collective-permute-start(bf16[8,64,128]{2,1,0:T(8,128)(2,1)S(1)} %get-tuple-element.59.refs_2_.refs_3_), channel_id=1, source_target_pairs={{0,16},{8,24},{16,0},{24,8},{1,17},{9,25},{17,1},{25,9},{2,18},{10... | collective-permute-start | bytes 393224 | tf_op jit(solution)/shard_map/ppermute | solution.py:39
  39.6 2.5 %collective-permute-start.17 = (bf16[8,64,128]{2,1,0:T(8,128)(2,1)S(1)}, bf16[8,64,128]{2,1,0:T(8,128)(2,1)S(1)}, u32[]{:S(2)}, u32[]{:S(2)}) collective-permute-start(bf16[8,64,128]{2,1,0:T(8,128)(2,1)S(1)} %get-tuple-element.59.refs_2_.refs_3_), channel_id=1, source_target_pairs={{0,6},{1,7},{2,4},{3,5},{4,2},{5,3},{6,0},{7,1},{8,14},{9,15},{10,... | collective-permute-start | bytes 393224 | tf_op jit(solution)/shard_map/ppermute | solution.py:39
  43.3 2.1 %collective-permute-done.24.refs_5_ = bf16[7,64,128]{2,1,0:T(8,128)(2,1)S(1)} collective-permute-done((bf16[7,64,128]{2,1,0:T(8,128)(2,1)S(1)}, bf16[7,64,128]{2,1,0:T(8,128)(2,1)S(1)}, u32[]{:S(2)}, u32[]{:S(2)}) %collective-permute-start.24) | collective-permute-done | bytes 114720 | tf_op jit(solution)/shard_map/ppermute | solution.py:39
  45.4 1.4 %collective-permute-start.26 = (bf16[9,64,128]{2,1,0:T(8,128)(2,1)S(1)}, bf16[9,64,128]{2,1,0:T(8,128)(2,1)S(1)}, u32[]{:S(2)}, u32[]{:S(2)}) collective-permute-start(bf16[9,64,128]{2,1,0:T(8,128)(2,1)S(1)} %pad_maximum_fusion.1), channel_id=1, source_target_pairs={{0,8},{8,0},{16,24},{24,16},{1,9},{9,1},{17,25},{25,17},{2,10},{10... | collective-permute-start | bytes 442376 | tf_op jit(solution)/shard_map/ppermute | solution.py:39
  49.3 1.0 %shard_map.67 = (f32[8,64,128]{2,1,0:T(8,128)S(1)}, f32[32,64,128]{2,1,0:T(8,128)S(1)}, bf16[512,128]{1,0:T(8,128)(2,1)S(1)}, bf16[512,128]{1,0:T(8,128)(2,1)S(1)}, bf16[512,128]{1,0:T(8,128)(2,1)S(1)}) custom-call(s32[3,32]{1,0:T(4,128)S(1)} %get-tuple-element.40.refs_0_.refs_1_, ...), custom_call_target="tpu_custom_call", output_to_operand_aliasing={{1}: (10, {})} | custom-call | flops 67108864 | bytes 3146112 | tf_op jit(solution)/shard_map/pallas_call | solution.py:25
  50.6 1.4 %shard_map.68 = (f32[64,64,128]{2,1,0:T(8,128)S(1)}, bf16[4,512,128]{2,1,0:T(8,128)(2,1)S(1)}) custom-call(f32[8,64,128]{2,1,0:T(8,128)S(1)} %get-tuple-element.61.refs_0_.refs_4_, s32[3,32]{1,0:T(4,128)S(1)} %get-tuple-element.40.refs_0_.refs_1_, bf16[32,128,128]{2,1,0:T(8,128)(2,1)S(1)} %shard_map.60.refs_1_.refs_2_, ...), custom_call_target="tpu_custom_call", output_to_operand_aliasing={{0}: (7, {})} | custom-call | flops 67108864 | bytes 3670400 | tf_op jit(solution)/shard_map/pallas_call | solution.py:25
  52.2 1.7 %collective-permute-start.31 = (bf16[512,128]{1,0:T(8,128)(2,1)S(1)}, bf16[512,128]{1,0:T(8,128)(2,1)S(1)}, u32[]{:S(2)}, u32[]{:S(2)}) collective-permute-start(bf16[512,128]{1,0:T(8,128)(2,1)S(1)} %get-tuple-element.71), channel_id=1, source_target_pairs={{0,8},{8,0},{16,24},{24,16},{1,9},{9,1},{17,25},{25,17},{2,10},{10... | collective-permute-start | bytes 393224 | tf_op jit(solution)/shard_map/ppermute | solution.py:39
  53.9 0.8 collective-permute-start.32
  54.8 1.9 %collective-permute-start.33 = (bf16[512,128]{1,0:T(8,128)(2,1)S(1)}, bf16[512,128]{1,0:T(8,128)(2,1)S(1)}, u32[]{:S(2)}, u32[]{:S(2)}) collective-permute-start(bf16[512,128]{1,0:T(8,128)(2,1)S(1)} %get-tuple-element.73), channel_id=1, source_target_pairs={{0,24},{8,16},{16,8},{24,0},{1,25},{9,17},{17,9},{25,1},{2,26},{10... | collective-permute-start | bytes 393224 | tf_op jit(solution)/shard_map/ppermute | solution.py:39
  56.8 2.5 %collective-permute-start.28 = (bf16[512,128]{1,0:T(8,128)(2,1)S(1)}, bf16[512,128]{1,0:T(8,128)(2,1)S(1)}, u32[]{:S(2)}, u32[]{:S(2)}) collective-permute-start(bf16[512,128]{1,0:T(8,128)(2,1)S(1)} %get-tuple-element.68), channel_id=1, source_target_pairs={{0,6},{1,7},{2,4},{3,5},{4,2},{5,3},{6,0},{7,1},{8,14},{9,15},{10,... | collective-permute-start | bytes 393224 | tf_op jit(solution)/shard_map/ppermute | solution.py:39
  59.8 1.6 %collective-permute-start.30 = (bf16[512,128]{1,0:T(8,128)(2,1)S(1)}, bf16[512,128]{1,0:T(8,128)(2,1)S(1)}, u32[]{:S(2)}, u32[]{:S(2)}) collective-permute-start(bf16[512,128]{1,0:T(8,128)(2,1)S(1)} %get-tuple-element.70), channel_id=1, source_target_pairs={{0,2},{1,3},{2,0},{3,1},{4,6},{5,7},{6,4},{7,5},{8,10},{9,11},{10,... | collective-permute-start | bytes 393224 | tf_op jit(solution)/shard_map/ppermute | solution.py:39
  61.4 5.4 %collective-permute-done.32.refs_9_ = bf16[512,128]{1,0:T(8,128)(2,1)S(1)} collective-permute-done((bf16[512,128]{1,0:T(8,128)(2,1)S(1)}, bf16[512,128]{1,0:T(8,128)(2,1)S(1)}, u32[]{:S(2)}, u32[]{:S(2)}) %collective-permute-start.32) | collective-permute-done | bytes 131104 | tf_op jit(solution)/shard_map/ppermute | solution.py:39
  67.0 2.6 %collective-permute-start.42 = (bf16[8,64,128]{2,1,0:T(8,128)(2,1)S(1)}, bf16[8,64,128]{2,1,0:T(8,128)(2,1)S(1)}, u32[]{:S(2)}, u32[]{:S(2)}) collective-permute-start(bf16[8,64,128]{2,1,0:T(8,128)(2,1)S(1)} %get-tuple-element.75.refs_2_.refs_3_), channel_id=1, source_target_pairs={{0,16},{8,24},{16,0},{24,8},{1,17},{9,25},{17,1},{25,9},{2,18},{10... | collective-permute-start | bytes 393224 | tf_op jit(solution)/shard_map/ppermute | solution.py:39
  69.7 2.5 %collective-permute-start.34 = (bf16[8,64,128]{2,1,0:T(8,128)(2,1)S(1)}, bf16[8,64,128]{2,1,0:T(8,128)(2,1)S(1)}, u32[]{:S(2)}, u32[]{:S(2)}) collective-permute-start(bf16[8,64,128]{2,1,0:T(8,128)(2,1)S(1)} %get-tuple-element.75.refs_2_.refs_3_), channel_id=1, source_target_pairs={{0,6},{1,7},{2,4},{3,5},{4,2},{5,3},{6,0},{7,1},{8,14},{9,15},{10,... | collective-permute-start | bytes 393224 | tf_op jit(solution)/shard_map/ppermute | solution.py:39
  73.9 1.4 %collective-permute-done.41.refs_5_ = bf16[7,64,128]{2,1,0:T(8,128)(2,1)S(1)} collective-permute-done((bf16[7,64,128]{2,1,0:T(8,128)(2,1)S(1)}, bf16[7,64,128]{2,1,0:T(8,128)(2,1)S(1)}, u32[]{:S(2)}, u32[]{:S(2)}) %collective-permute-start.41) | collective-permute-done | bytes 114720 | tf_op jit(solution)/shard_map/ppermute | solution.py:39
  75.7 1.0 collective-permute-start.43
  78.4 0.8 collective-permute-done.39.refs_8_
  79.4 1.0 shard_map.71.refs_1_
  80.9 1.2 %shard_map.73 = f32[40,128]{1,0:T(8,128)S(1)} custom-call(s32[3,32]{1,0:T(4,128)S(1)} %get-tuple-element.40.refs_0_.refs_1_, bf16[64,4096]{1,0:T(8,128)(2,1)S(1)} %shard_map.71.refs_1_, f32[64,128]{1,0:T(8,128)S(1)} %shard_map.72.refs_2_, bf16[8,64,128]{2,1,0:T(8,128)(2,1)S(1)} %get-tuple-element.75.refs_2_.refs_3_, ...), custom_call_target="tpu_custom_call" | custom-call | flops 33554432 | bytes 1081728 | tf_op jit(solution)/shard_map/pallas_call | solution.py:25
  82.2 1.2 %collective-permute-done.44 = f32[40,128]{1,0:T(8,128)S(1)} collective-permute-done((f32[40,128]{1,0:T(8,128)S(1)}, f32[40,128]{1,0:T(8,128)S(1)}, u32[]{:S(2)}, u32[]{:S(2)}) %collective-permute-start.44) | collective-permute-done | bytes 20512 | tf_op jit(solution)/shard_map/ppermute | solution.py:39
  83.4 2.0 %collective-permute-start.45 = (f32[40,128]{1,0:T(8,128)S(1)}, f32[40,128]{1,0:T(8,128)S(1)}, u32[]{:S(2)}, u32[]{:S(2)}) collective-permute-start(f32[40,128]{1,0:T(8,128)S(1)} %add.12), channel_id=1, source_target_pairs={{0,6},{1,7},{2,4},{3,5},{4,2},{5,3},{6,0},{7,1},{8,14},{9,15},{10,... | collective-permute-start | bytes 61448 | tf_op jit(solution)/shard_map/ppermute | solution.py:39
  85.4 0.9 collective-permute-start.46
  86.9 1.2 %collective-permute-done.45 = f32[40,128]{1,0:T(8,128)S(1)} collective-permute-done((f32[40,128]{1,0:T(8,128)S(1)}, f32[40,128]{1,0:T(8,128)S(1)}, u32[]{:S(2)}, u32[]{:S(2)}) %collective-permute-start.45) | collective-permute-done | bytes 20512 | tf_op jit(solution)/shard_map/ppermute | solution.py:39
  88.1 1.1 %collective-permute-done.46 = f32[40,128]{1,0:T(8,128)S(1)} collective-permute-done((f32[40,128]{1,0:T(8,128)S(1)}, f32[40,128]{1,0:T(8,128)S(1)}, u32[]{:S(2)}, u32[]{:S(2)}) %collective-permute-start.46) | collective-permute-done | bytes 20512 | tf_op jit(solution)/shard_map/ppermute | solution.py:39
  89.2 0.9 collective-permute-done.47
  90.1 1.9 %collective-permute-start.48 = (f32[40,128]{1,0:T(8,128)S(1)}, f32[40,128]{1,0:T(8,128)S(1)}, u32[]{:S(2)}, u32[]{:S(2)}) collective-permute-start(f32[40,128]{1,0:T(8,128)S(1)} %add_add_fusion.refs_1_), channel_id=1, source_target_pairs={{0,24},{8,16},{16,8},{24,0},{1,25},{9,17},{17,9},{25,1},{2,26},{10... | collective-permute-start | bytes 61448 | tf_op jit(solution)/shard_map/ppermute | solution.py:39
  92.0 0.9 collective-permute-start.49
  92.8 1.7 %collective-permute-start.50 = (f32[40,128]{1,0:T(8,128)S(1)}, f32[40,128]{1,0:T(8,128)S(1)}, u32[]{:S(2)}, u32[]{:S(2)}) collective-permute-start(f32[40,128]{1,0:T(8,128)S(1)} %add_add_fusion.refs_1_), channel_id=1, source_target_pairs={{0,8},{8,0},{16,24},{24,16},{1,9},{9,1},{17,25},{25,17},{2,10},{10... | collective-permute-start | bytes 61448 | tf_op jit(solution)/shard_map/ppermute | solution.py:39
  94.5 1.2 %collective-permute-done.48.refs_2_ = f32[40,128]{1,0:T(8,128)S(1)} collective-permute-done((f32[40,128]{1,0:T(8,128)S(1)}, f32[40,128]{1,0:T(8,128)S(1)}, u32[]{:S(2)}, u32[]{:S(2)}) %collective-permute-start.48) | collective-permute-done | bytes 20512 | tf_op jit(solution)/shard_map/ppermute | solution.py:39
  95.7 1.1 %collective-permute-done.49.refs_3_ = f32[40,128]{1,0:T(8,128)S(1)} collective-permute-done((f32[40,128]{1,0:T(8,128)S(1)}, f32[40,128]{1,0:T(8,128)S(1)}, u32[]{:S(2)}, u32[]{:S(2)}) %collective-permute-start.49) | collective-permute-done | bytes 20512 | tf_op jit(solution)/shard_map/ppermute | solution.py:39
  96.9 3.8 %shard_map.74 = (f32[64,1024]{1,0:T(8,128)}, f32[64,64]{1,0:T(8,128)}) custom-call(f32[64,1024]{1,0:T(8,128)S(1)} %get-tuple-element.74.refs_0_, f32[40,128]{1,0:T(8,128)S(1)} %add_add_fusion.refs_1_, f32[40,128]{1,0:T(8,128)S(1)} %collective-permute-done.48.refs_2_, f32[40,128]{1,0:T(8,128)S(1)} %collective-permute-done.49.refs_3_, ...), custom_call_target="tpu_custom_call" | custom-call | bytes 344064 | tf_op jit(solution)/shard_map/pallas_call | solution.py:25
  (93 shorter events, 15.2 us)
Async XLA Ops:
  3.1 10.6 %collective-permute-start.8 = (bf16[8,64,128]{2,1,0:T(8,128)(2,1)S(1)}, bf16[8,64,128]{2,1,0:T(8,128)(2,1)S(1)}, u32[]{:S(2)}, u32[]{:S(2)}) collective-permute-start(bf16[8,64,128]{2,1,0:T(8,128)(2,1)S(1)} %get-tuple-element.41.refs_2_.refs_3_), channel_id=1, source_target_pairs={{0,16},{8,24},{16,0},{24,8},{1,17},{9,25},{17,1},{25,9},{2,18},{10... | collective-permute-start | bytes 393224 | tf_op jit(solution)/shard_map/ppermute | solution.py:39
  7.2 6.5 %collective-permute-start.7 = (bf16[7,64,128]{2,1,0:T(8,128)(2,1)S(1)}, bf16[7,64,128]{2,1,0:T(8,128)(2,1)S(1)}, u32[]{:S(2)}, u32[]{:S(2)}) collective-permute-start(bf16[7,64,128]{2,1,0:T(8,128)(2,1)S(1)} %slice.18), channel_id=1, source_target_pairs={{0,8},{8,0},{16,24},{24,16},{1,9},{9,1},{17,25},{25,17},{2,10},{10... | collective-permute-start | bytes 344072 | tf_op jit(solution)/shard_map/ppermute | solution.py:39
  8.8 6.6 %collective-permute-start = (bf16[8,64,128]{2,1,0:T(8,128)(2,1)S(1)}, bf16[8,64,128]{2,1,0:T(8,128)(2,1)S(1)}, u32[]{:S(2)}, u32[]{:S(2)}) collective-permute-start(bf16[8,64,128]{2,1,0:T(8,128)(2,1)S(1)} %get-tuple-element.41.refs_2_.refs_3_), channel_id=1, source_target_pairs={{0,6},{1,7},{2,4},{3,5},{4,2},{5,3},{6,0},{7,1},{8,14},{9,15},{10,... | collective-permute-start | bytes 393224 | tf_op jit(solution)/shard_map/ppermute | solution.py:39
  11.3 5.9 %collective-permute-start.1 = (bf16[8,64,128]{2,1,0:T(8,128)(2,1)S(1)}, bf16[8,64,128]{2,1,0:T(8,128)(2,1)S(1)}, u32[]{:S(2)}, u32[]{:S(2)}) collective-permute-start(bf16[8,64,128]{2,1,0:T(8,128)(2,1)S(1)} %get-tuple-element.41.refs_2_.refs_3_), channel_id=1, source_target_pairs={{0,4},{1,5},{2,6},{3,7},{4,0},{5,1},{6,2},{7,3},{8,12},{9,13},{10,... | collective-permute-start | bytes 393224 | tf_op jit(solution)/shard_map/ppermute | solution.py:39
  11.8 5.5 %collective-permute-start.2 = (bf16[8,64,128]{2,1,0:T(8,128)(2,1)S(1)}, bf16[8,64,128]{2,1,0:T(8,128)(2,1)S(1)}, u32[]{:S(2)}, u32[]{:S(2)}) collective-permute-start(bf16[8,64,128]{2,1,0:T(8,128)(2,1)S(1)} %get-tuple-element.41.refs_2_.refs_3_), channel_id=1, source_target_pairs={{0,2},{1,3},{2,0},{3,1},{4,6},{5,7},{6,4},{7,5},{8,10},{9,11},{10,... | collective-permute-start | bytes 393224 | tf_op jit(solution)/shard_map/ppermute | solution.py:39
  13.7 6.5 %collective-permute-start.9 = (bf16[9,64,128]{2,1,0:T(8,128)(2,1)S(1)}, bf16[9,64,128]{2,1,0:T(8,128)(2,1)S(1)}, u32[]{:S(2)}, u32[]{:S(2)}) collective-permute-start(bf16[9,64,128]{2,1,0:T(8,128)(2,1)S(1)} %pad_maximum_fusion), channel_id=1, source_target_pairs={{0,8},{8,0},{16,24},{24,16},{1,9},{9,1},{17,25},{25,17},{2,10},{10... | collective-permute-start | bytes 442376 | tf_op jit(solution)/shard_map/ppermute | solution.py:39
  15.0 4.1 %collective-permute-start.3 = (bf16[8,64,128]{2,1,0:T(8,128)(2,1)S(1)}, bf16[8,64,128]{2,1,0:T(8,128)(2,1)S(1)}, u32[]{:S(2)}, u32[]{:S(2)}) collective-permute-start(bf16[8,64,128]{2,1,0:T(8,128)(2,1)S(1)} %get-tuple-element.41.refs_2_.refs_3_), channel_id=1, source_target_pairs={{0,1},{1,0},{2,3},{3,2},{4,5},{5,4},{6,7},{7,6},{8,9},{9,8},{10,11... | collective-permute-start | bytes 393224 | tf_op jit(solution)/shard_map/ppermute | solution.py:39
  15.4 3.7 %collective-permute-start.4 = (bf16[8,64,128]{2,1,0:T(8,128)(2,1)S(1)}, bf16[8,64,128]{2,1,0:T(8,128)(2,1)S(1)}, u32[]{:S(2)}, u32[]{:S(2)}) collective-permute-start(bf16[8,64,128]{2,1,0:T(8,128)(2,1)S(1)} %collective-permute-done.refs_3_), channel_id=1, source_target_pairs={{0,1},{1,0},{2,3},{3,2},{4,5},{5,4},{6,7},{7,6},{8,9},{9,8},{10,11... | collective-permute-start | bytes 393224 | tf_op jit(solution)/shard_map/ppermute | solution.py:39
  17.2 1.8 %collective-permute-start.5 = (bf16[8,64,128]{2,1,0:T(8,128)(2,1)S(1)}, bf16[8,64,128]{2,1,0:T(8,128)(2,1)S(1)}, u32[]{:S(2)}, u32[]{:S(2)}) collective-permute-start(bf16[8,64,128]{2,1,0:T(8,128)(2,1)S(1)} %collective-permute-done.1.refs_4_), channel_id=1, source_target_pairs={{0,1},{1,0},{2,3},{3,2},{4,5},{5,4},{6,7},{7,6},{8,9},{9,8},{10,11... | collective-permute-start | bytes 393224 | tf_op jit(solution)/shard_map/ppermute | solution.py:39
  17.3 1.8 %collective-permute-start.6 = (bf16[8,64,128]{2,1,0:T(8,128)(2,1)S(1)}, bf16[8,64,128]{2,1,0:T(8,128)(2,1)S(1)}, u32[]{:S(2)}, u32[]{:S(2)}) collective-permute-start(bf16[8,64,128]{2,1,0:T(8,128)(2,1)S(1)} %collective-permute-done.2.refs_5_), channel_id=1, source_target_pairs={{0,1},{1,0},{2,3},{3,2},{4,5},{5,4},{6,7},{7,6},{8,9},{9,8},{10,11... | collective-permute-start | bytes 393224 | tf_op jit(solution)/shard_map/ppermute | solution.py:39
  21.7 4.5 %collective-permute-start.10 = (bf16[4,528,128]{2,1,0:T(8,128)(2,1)S(1)}, bf16[4,528,128]{2,1,0:T(8,128)(2,1)S(1)}, u32[]{:S(2)}, u32[]{:S(2)}) collective-permute-start(bf16[4,528,128]{2,1,0:T(8,128)(2,1)S(1)} %get-tuple-element.48), channel_id=1, source_target_pairs={{0,1},{1,0},{2,3},{3,2},{4,5},{5,4},{6,7},{7,6},{8,9},{9,8},{10,11... | collective-permute-start | bytes 1622024 | tf_op jit(solution)/shard_map/ppermute | solution.py:39
  21.9 8.4 %collective-permute-start.14 = (bf16[528,128]{1,0:T(8,128)(2,1)S(1)}, bf16[528,128]{1,0:T(8,128)(2,1)S(1)}, u32[]{:S(2)}, u32[]{:S(2)}) collective-permute-start(bf16[528,128]{1,0:T(8,128)(2,1)S(1)} %get-tuple-element.54), channel_id=1, source_target_pairs={{0,8},{8,0},{16,24},{24,16},{1,9},{9,1},{17,25},{25,17},{2,10},{10... | collective-permute-start | bytes 405512 | tf_op jit(solution)/shard_map/ppermute | solution.py:39
  22.4 13.2 %collective-permute-start.15 = (bf16[528,128]{1,0:T(8,128)(2,1)S(1)}, bf16[528,128]{1,0:T(8,128)(2,1)S(1)}, u32[]{:S(2)}, u32[]{:S(2)}) collective-permute-start(bf16[528,128]{1,0:T(8,128)(2,1)S(1)} %get-tuple-element.55), channel_id=1, source_target_pairs={{0,16},{8,24},{16,0},{24,8},{1,17},{9,25},{17,1},{25,9},{2,18},{10... | collective-permute-start | bytes 405512 | tf_op jit(solution)/shard_map/ppermute | solution.py:39
  25.1 10.4 %collective-permute-start.16 = (bf16[528,128]{1,0:T(8,128)(2,1)S(1)}, bf16[528,128]{1,0:T(8,128)(2,1)S(1)}, u32[]{:S(2)}, u32[]{:S(2)}) collective-permute-start(bf16[528,128]{1,0:T(8,128)(2,1)S(1)} %get-tuple-element.56), channel_id=1, source_target_pairs={{0,24},{8,16},{16,8},{24,0},{1,25},{9,17},{17,9},{25,1},{2,26},{10... | collective-permute-start | bytes 405512 | tf_op jit(solution)/shard_map/ppermute | solution.py:39
  26.4 9.1 %collective-permute-start.11 = (bf16[528,128]{1,0:T(8,128)(2,1)S(1)}, bf16[528,128]{1,0:T(8,128)(2,1)S(1)}, u32[]{:S(2)}, u32[]{:S(2)}) collective-permute-start(bf16[528,128]{1,0:T(8,128)(2,1)S(1)} %get-tuple-element.51), channel_id=1, source_target_pairs={{0,6},{1,7},{2,4},{3,5},{4,2},{5,3},{6,0},{7,1},{8,14},{9,15},{10,... | collective-permute-start | bytes 405512 | tf_op jit(solution)/shard_map/ppermute | solution.py:39
  28.2 7.3 %collective-permute-start.12 = (bf16[528,128]{1,0:T(8,128)(2,1)S(1)}, bf16[528,128]{1,0:T(8,128)(2,1)S(1)}, u32[]{:S(2)}, u32[]{:S(2)}) collective-permute-start(bf16[528,128]{1,0:T(8,128)(2,1)S(1)} %get-tuple-element.52), channel_id=1, source_target_pairs={{0,4},{1,5},{2,6},{3,7},{4,0},{5,1},{6,2},{7,3},{8,12},{9,13},{10,... | collective-permute-start | bytes 405512 | tf_op jit(solution)/shard_map/ppermute | solution.py:39
  30.3 5.3 %collective-permute-start.13 = (bf16[528,128]{1,0:T(8,128)(2,1)S(1)}, bf16[528,128]{1,0:T(8,128)(2,1)S(1)}, u32[]{:S(2)}, u32[]{:S(2)}) collective-permute-start(bf16[528,128]{1,0:T(8,128)(2,1)S(1)} %get-tuple-element.53), channel_id=1, source_target_pairs={{0,2},{1,3},{2,0},{3,1},{4,6},{5,7},{6,4},{7,5},{8,10},{9,11},{10,... | collective-permute-start | bytes 405512 | tf_op jit(solution)/shard_map/ppermute | solution.py:39
  35.7 9.7 %collective-permute-start.25 = (bf16[8,64,128]{2,1,0:T(8,128)(2,1)S(1)}, bf16[8,64,128]{2,1,0:T(8,128)(2,1)S(1)}, u32[]{:S(2)}, u32[]{:S(2)}) collective-permute-start(bf16[8,64,128]{2,1,0:T(8,128)(2,1)S(1)} %get-tuple-element.59.refs_2_.refs_3_), channel_id=1, source_target_pairs={{0,16},{8,24},{16,0},{24,8},{1,17},{9,25},{17,1},{25,9},{2,18},{10... | collective-permute-start | bytes 393224 | tf_op jit(solution)/shard_map/ppermute | solution.py:39
  39.5 5.9 %collective-permute-start.24 = (bf16[7,64,128]{2,1,0:T(8,128)(2,1)S(1)}, bf16[7,64,128]{2,1,0:T(8,128)(2,1)S(1)}, u32[]{:S(2)}, u32[]{:S(2)}) collective-permute-start(bf16[7,64,128]{2,1,0:T(8,128)(2,1)S(1)} %slice.20), channel_id=1, source_target_pairs={{0,8},{8,0},{16,24},{24,16},{1,9},{9,1},{17,25},{25,17},{2,10},{10... | collective-permute-start | bytes 344072 | tf_op jit(solution)/shard_map/ppermute | solution.py:39
  39.6 7.2 %collective-permute-start.17 = (bf16[8,64,128]{2,1,0:T(8,128)(2,1)S(1)}, bf16[8,64,128]{2,1,0:T(8,128)(2,1)S(1)}, u32[]{:S(2)}, u32[]{:S(2)}) collective-permute-start(bf16[8,64,128]{2,1,0:T(8,128)(2,1)S(1)} %get-tuple-element.59.refs_2_.refs_3_), channel_id=1, source_target_pairs={{0,6},{1,7},{2,4},{3,5},{4,2},{5,3},{6,0},{7,1},{8,14},{9,15},{10,... | collective-permute-start | bytes 393224 | tf_op jit(solution)/shard_map/ppermute | solution.py:39
  42.1 5.7 %collective-permute-start.18 = (bf16[8,64,128]{2,1,0:T(8,128)(2,1)S(1)}, bf16[8,64,128]{2,1,0:T(8,128)(2,1)S(1)}, u32[]{:S(2)}, u32[]{:S(2)}) collective-permute-start(bf16[8,64,128]{2,1,0:T(8,128)(2,1)S(1)} %get-tuple-element.59.refs_2_.refs_3_), channel_id=1, source_target_pairs={{0,4},{1,5},{2,6},{3,7},{4,0},{5,1},{6,2},{7,3},{8,12},{9,13},{10,... | collective-permute-start | bytes 393224 | tf_op jit(solution)/shard_map/ppermute | solution.py:39
  42.6 5.3 %collective-permute-start.19 = (bf16[8,64,128]{2,1,0:T(8,128)(2,1)S(1)}, bf16[8,64,128]{2,1,0:T(8,128)(2,1)S(1)}, u32[]{:S(2)}, u32[]{:S(2)}) collective-permute-start(bf16[8,64,128]{2,1,0:T(8,128)(2,1)S(1)} %get-tuple-element.59.refs_2_.refs_3_), channel_id=1, source_target_pairs={{0,2},{1,3},{2,0},{3,1},{4,6},{5,7},{6,4},{7,5},{8,10},{9,11},{10,... | collective-permute-start | bytes 393224 | tf_op jit(solution)/shard_map/ppermute | solution.py:39
  45.4 5.2 %collective-permute-start.26 = (bf16[9,64,128]{2,1,0:T(8,128)(2,1)S(1)}, bf16[9,64,128]{2,1,0:T(8,128)(2,1)S(1)}, u32[]{:S(2)}, u32[]{:S(2)}) collective-permute-start(bf16[9,64,128]{2,1,0:T(8,128)(2,1)S(1)} %pad_maximum_fusion.1), channel_id=1, source_target_pairs={{0,8},{8,0},{16,24},{24,16},{1,9},{9,1},{17,25},{25,17},{2,10},{10... | collective-permute-start | bytes 442376 | tf_op jit(solution)/shard_map/ppermute | solution.py:39
  46.8 1.5 %collective-permute-start.20 = (bf16[8,64,128]{2,1,0:T(8,128)(2,1)S(1)}, bf16[8,64,128]{2,1,0:T(8,128)(2,1)S(1)}, u32[]{:S(2)}, u32[]{:S(2)}) collective-permute-start(bf16[8,64,128]{2,1,0:T(8,128)(2,1)S(1)} %get-tuple-element.59.refs_2_.refs_3_), channel_id=1, source_target_pairs={{0,1},{1,0},{2,3},{3,2},{4,5},{5,4},{6,7},{7,6},{8,9},{9,8},{10,11... | collective-permute-start | bytes 393224 | tf_op jit(solution)/shard_map/ppermute | solution.py:39
  46.8 1.5 %collective-permute-start.21 = (bf16[8,64,128]{2,1,0:T(8,128)(2,1)S(1)}, bf16[8,64,128]{2,1,0:T(8,128)(2,1)S(1)}, u32[]{:S(2)}, u32[]{:S(2)}) collective-permute-start(bf16[8,64,128]{2,1,0:T(8,128)(2,1)S(1)} %collective-permute-done.17.refs_3_), channel_id=1, source_target_pairs={{0,1},{1,0},{2,3},{3,2},{4,5},{5,4},{6,7},{7,6},{8,9},{9,8},{10,11... | collective-permute-start | bytes 393224 | tf_op jit(solution)/shard_map/ppermute | solution.py:39
  47.9 1.4 %collective-permute-start.23 = (bf16[8,64,128]{2,1,0:T(8,128)(2,1)S(1)}, bf16[8,64,128]{2,1,0:T(8,128)(2,1)S(1)}, u32[]{:S(2)}, u32[]{:S(2)}) collective-permute-start(bf16[8,64,128]{2,1,0:T(8,128)(2,1)S(1)} %collective-permute-done.19.refs_5_), channel_id=1, source_target_pairs={{0,1},{1,0},{2,3},{3,2},{4,5},{5,4},{6,7},{7,6},{8,9},{9,8},{10,11... | collective-permute-start | bytes 393224 | tf_op jit(solution)/shard_map/ppermute | solution.py:39
  52.1 4.6 %collective-permute-start.27 = (bf16[4,512,128]{2,1,0:T(8,128)(2,1)S(1)}, bf16[4,512,128]{2,1,0:T(8,128)(2,1)S(1)}, u32[]{:S(2)}, u32[]{:S(2)}) collective-permute-start(bf16[4,512,128]{2,1,0:T(8,128)(2,1)S(1)} %get-tuple-element.66), channel_id=1, source_target_pairs={{0,1},{1,0},{2,3},{3,2},{4,5},{5,4},{6,7},{7,6},{8,9},{9,8},{10,11... | collective-permute-start | bytes 1572872 | tf_op jit(solution)/shard_map/ppermute | solution.py:39
  52.2 7.5 %collective-permute-start.31 = (bf16[512,128]{1,0:T(8,128)(2,1)S(1)}, bf16[512,128]{1,0:T(8,128)(2,1)S(1)}, u32[]{:S(2)}, u32[]{:S(2)}) collective-permute-start(bf16[512,128]{1,0:T(8,128)(2,1)S(1)} %get-tuple-element.71), channel_id=1, source_target_pairs={{0,8},{8,0},{16,24},{24,16},{1,9},{9,1},{17,25},{25,17},{2,10},{10... | collective-permute-start | bytes 393224 | tf_op jit(solution)/shard_map/ppermute | solution.py:39
  53.9 12.9 %collective-permute-start.32 = (bf16[512,128]{1,0:T(8,128)(2,1)S(1)}, bf16[512,128]{1,0:T(8,128)(2,1)S(1)}, u32[]{:S(2)}, u32[]{:S(2)}) collective-permute-start(bf16[512,128]{1,0:T(8,128)(2,1)S(1)} %get-tuple-element.72), channel_id=1, source_target_pairs={{0,16},{8,24},{16,0},{24,8},{1,17},{9,25},{17,1},{25,9},{2,18},{10... | collective-permute-start | bytes 393224 | tf_op jit(solution)/shard_map/ppermute | solution.py:39
  54.8 12.0 %collective-permute-start.33 = (bf16[512,128]{1,0:T(8,128)(2,1)S(1)}, bf16[512,128]{1,0:T(8,128)(2,1)S(1)}, u32[]{:S(2)}, u32[]{:S(2)}) collective-permute-start(bf16[512,128]{1,0:T(8,128)(2,1)S(1)} %get-tuple-element.73), channel_id=1, source_target_pairs={{0,24},{8,16},{16,8},{24,0},{1,25},{9,17},{17,9},{25,1},{2,26},{10... | collective-permute-start | bytes 393224 | tf_op jit(solution)/shard_map/ppermute | solution.py:39
  56.8 10.1 %collective-permute-start.28 = (bf16[512,128]{1,0:T(8,128)(2,1)S(1)}, bf16[512,128]{1,0:T(8,128)(2,1)S(1)}, u32[]{:S(2)}, u32[]{:S(2)}) collective-permute-start(bf16[512,128]{1,0:T(8,128)(2,1)S(1)} %get-tuple-element.68), channel_id=1, source_target_pairs={{0,6},{1,7},{2,4},{3,5},{4,2},{5,3},{6,0},{7,1},{8,14},{9,15},{10,... | collective-permute-start | bytes 393224 | tf_op jit(solution)/shard_map/ppermute | solution.py:39
  59.3 7.6 %collective-permute-start.29 = (bf16[512,128]{1,0:T(8,128)(2,1)S(1)}, bf16[512,128]{1,0:T(8,128)(2,1)S(1)}, u32[]{:S(2)}, u32[]{:S(2)}) collective-permute-start(bf16[512,128]{1,0:T(8,128)(2,1)S(1)} %get-tuple-element.69), channel_id=1, source_target_pairs={{0,4},{1,5},{2,6},{3,7},{4,0},{5,1},{6,2},{7,3},{8,12},{9,13},{10,... | collective-permute-start | bytes 393224 | tf_op jit(solution)/shard_map/ppermute | solution.py:39
  59.8 7.1 %collective-permute-start.30 = (bf16[512,128]{1,0:T(8,128)(2,1)S(1)}, bf16[512,128]{1,0:T(8,128)(2,1)S(1)}, u32[]{:S(2)}, u32[]{:S(2)}) collective-permute-start(bf16[512,128]{1,0:T(8,128)(2,1)S(1)} %get-tuple-element.70), channel_id=1, source_target_pairs={{0,2},{1,3},{2,0},{3,1},{4,6},{5,7},{6,4},{7,5},{8,10},{9,11},{10,... | collective-permute-start | bytes 393224 | tf_op jit(solution)/shard_map/ppermute | solution.py:39
  67.0 8.7 %collective-permute-start.42 = (bf16[8,64,128]{2,1,0:T(8,128)(2,1)S(1)}, bf16[8,64,128]{2,1,0:T(8,128)(2,1)S(1)}, u32[]{:S(2)}, u32[]{:S(2)}) collective-permute-start(bf16[8,64,128]{2,1,0:T(8,128)(2,1)S(1)} %get-tuple-element.75.refs_2_.refs_3_), channel_id=1, source_target_pairs={{0,16},{8,24},{16,0},{24,8},{1,17},{9,25},{17,1},{25,9},{2,18},{10... | collective-permute-start | bytes 393224 | tf_op jit(solution)/shard_map/ppermute | solution.py:39
  69.6 5.7 %collective-permute-start.41 = (bf16[7,64,128]{2,1,0:T(8,128)(2,1)S(1)}, bf16[7,64,128]{2,1,0:T(8,128)(2,1)S(1)}, u32[]{:S(2)}, u32[]{:S(2)}) collective-permute-start(bf16[7,64,128]{2,1,0:T(8,128)(2,1)S(1)} %slice.22), channel_id=1, source_target_pairs={{0,8},{8,0},{16,24},{24,16},{1,9},{9,1},{17,25},{25,17},{2,10},{10... | collective-permute-start | bytes 344072 | tf_op jit(solution)/shard_map/ppermute | solution.py:39
  69.7 7.0 %collective-permute-start.34 = (bf16[8,64,128]{2,1,0:T(8,128)(2,1)S(1)}, bf16[8,64,128]{2,1,0:T(8,128)(2,1)S(1)}, u32[]{:S(2)}, u32[]{:S(2)}) collective-permute-start(bf16[8,64,128]{2,1,0:T(8,128)(2,1)S(1)} %get-tuple-element.75.refs_2_.refs_3_), channel_id=1, source_target_pairs={{0,6},{1,7},{2,4},{3,5},{4,2},{5,3},{6,0},{7,1},{8,14},{9,15},{10,... | collective-permute-start | bytes 393224 | tf_op jit(solution)/shard_map/ppermute | solution.py:39
  72.3 5.6 %collective-permute-start.35 = (bf16[8,64,128]{2,1,0:T(8,128)(2,1)S(1)}, bf16[8,64,128]{2,1,0:T(8,128)(2,1)S(1)}, u32[]{:S(2)}, u32[]{:S(2)}) collective-permute-start(bf16[8,64,128]{2,1,0:T(8,128)(2,1)S(1)} %get-tuple-element.75.refs_2_.refs_3_), channel_id=1, source_target_pairs={{0,4},{1,5},{2,6},{3,7},{4,0},{5,1},{6,2},{7,3},{8,12},{9,13},{10,... | collective-permute-start | bytes 393224 | tf_op jit(solution)/shard_map/ppermute | solution.py:39
  72.8 5.2 %collective-permute-start.36 = (bf16[8,64,128]{2,1,0:T(8,128)(2,1)S(1)}, bf16[8,64,128]{2,1,0:T(8,128)(2,1)S(1)}, u32[]{:S(2)}, u32[]{:S(2)}) collective-permute-start(bf16[8,64,128]{2,1,0:T(8,128)(2,1)S(1)} %get-tuple-element.75.refs_2_.refs_3_), channel_id=1, source_target_pairs={{0,2},{1,3},{2,0},{3,1},{4,6},{5,7},{6,4},{7,5},{8,10},{9,11},{10,... | collective-permute-start | bytes 393224 | tf_op jit(solution)/shard_map/ppermute | solution.py:39
  75.7 5.2 %collective-permute-start.43 = (bf16[9,64,128]{2,1,0:T(8,128)(2,1)S(1)}, bf16[9,64,128]{2,1,0:T(8,128)(2,1)S(1)}, u32[]{:S(2)}, u32[]{:S(2)}) collective-permute-start(bf16[9,64,128]{2,1,0:T(8,128)(2,1)S(1)} %pad_maximum_fusion.2), channel_id=1, source_target_pairs={{0,8},{8,0},{16,24},{24,16},{1,9},{9,1},{17,25},{25,17},{2,10},{10... | collective-permute-start | bytes 442376 | tf_op jit(solution)/shard_map/ppermute | solution.py:39
  76.7 1.7 %collective-permute-start.37 = (bf16[8,64,128]{2,1,0:T(8,128)(2,1)S(1)}, bf16[8,64,128]{2,1,0:T(8,128)(2,1)S(1)}, u32[]{:S(2)}, u32[]{:S(2)}) collective-permute-start(bf16[8,64,128]{2,1,0:T(8,128)(2,1)S(1)} %get-tuple-element.75.refs_2_.refs_3_), channel_id=1, source_target_pairs={{0,1},{1,0},{2,3},{3,2},{4,5},{5,4},{6,7},{7,6},{8,9},{9,8},{10,11... | collective-permute-start | bytes 393224 | tf_op jit(solution)/shard_map/ppermute | solution.py:39
  76.7 1.7 %collective-permute-start.38 = (bf16[8,64,128]{2,1,0:T(8,128)(2,1)S(1)}, bf16[8,64,128]{2,1,0:T(8,128)(2,1)S(1)}, u32[]{:S(2)}, u32[]{:S(2)}) collective-permute-start(bf16[8,64,128]{2,1,0:T(8,128)(2,1)S(1)} %collective-permute-done.34.refs_3_), channel_id=1, source_target_pairs={{0,1},{1,0},{2,3},{3,2},{4,5},{5,4},{6,7},{7,6},{8,9},{9,8},{10,11... | collective-permute-start | bytes 393224 | tf_op jit(solution)/shard_map/ppermute | solution.py:39
  77.9 1.4 %collective-permute-start.40 = (bf16[8,64,128]{2,1,0:T(8,128)(2,1)S(1)}, bf16[8,64,128]{2,1,0:T(8,128)(2,1)S(1)}, u32[]{:S(2)}, u32[]{:S(2)}) collective-permute-start(bf16[8,64,128]{2,1,0:T(8,128)(2,1)S(1)} %collective-permute-done.36.refs_5_), channel_id=1, source_target_pairs={{0,1},{1,0},{2,3},{3,2},{4,5},{5,4},{6,7},{7,6},{8,9},{9,8},{10,11... | collective-permute-start | bytes 393224 | tf_op jit(solution)/shard_map/ppermute | solution.py:39
  83.4 4.7 %collective-permute-start.45 = (f32[40,128]{1,0:T(8,128)S(1)}, f32[40,128]{1,0:T(8,128)S(1)}, u32[]{:S(2)}, u32[]{:S(2)}) collective-permute-start(f32[40,128]{1,0:T(8,128)S(1)} %add.12), channel_id=1, source_target_pairs={{0,6},{1,7},{2,4},{3,5},{4,2},{5,3},{6,0},{7,1},{8,14},{9,15},{10,... | collective-permute-start | bytes 61448 | tf_op jit(solution)/shard_map/ppermute | solution.py:39
  85.4 3.8 %collective-permute-start.46 = (f32[40,128]{1,0:T(8,128)S(1)}, f32[40,128]{1,0:T(8,128)S(1)}, u32[]{:S(2)}, u32[]{:S(2)}) collective-permute-start(f32[40,128]{1,0:T(8,128)S(1)} %add.12), channel_id=1, source_target_pairs={{0,4},{1,5},{2,6},{3,7},{4,0},{5,1},{6,2},{7,3},{8,12},{9,13},{10,... | collective-permute-start | bytes 61448 | tf_op jit(solution)/shard_map/ppermute | solution.py:39
  86.3 3.8 %collective-permute-start.47 = (f32[40,128]{1,0:T(8,128)S(1)}, f32[40,128]{1,0:T(8,128)S(1)}, u32[]{:S(2)}, u32[]{:S(2)}) collective-permute-start(f32[40,128]{1,0:T(8,128)S(1)} %add.12), channel_id=1, source_target_pairs={{0,2},{1,3},{2,0},{3,1},{4,6},{5,7},{6,4},{7,5},{8,10},{9,11},{10,... | collective-permute-start | bytes 61448 | tf_op jit(solution)/shard_map/ppermute | solution.py:39
  90.1 5.6 %collective-permute-start.48 = (f32[40,128]{1,0:T(8,128)S(1)}, f32[40,128]{1,0:T(8,128)S(1)}, u32[]{:S(2)}, u32[]{:S(2)}) collective-permute-start(f32[40,128]{1,0:T(8,128)S(1)} %add_add_fusion.refs_1_), channel_id=1, source_target_pairs={{0,24},{8,16},{16,8},{24,0},{1,25},{9,17},{17,9},{25,1},{2,26},{10... | collective-permute-start | bytes 61448 | tf_op jit(solution)/shard_map/ppermute | solution.py:39
  92.0 4.9 %collective-permute-start.49 = (f32[40,128]{1,0:T(8,128)S(1)}, f32[40,128]{1,0:T(8,128)S(1)}, u32[]{:S(2)}, u32[]{:S(2)}) collective-permute-start(f32[40,128]{1,0:T(8,128)S(1)} %add_add_fusion.refs_1_), channel_id=1, source_target_pairs={{0,16},{8,24},{16,0},{24,8},{1,17},{9,25},{17,1},{25,9},{2,18},{10... | collective-permute-start | bytes 61448 | tf_op jit(solution)/shard_map/ppermute | solution.py:39
  92.8 4.0 %collective-permute-start.50 = (f32[40,128]{1,0:T(8,128)S(1)}, f32[40,128]{1,0:T(8,128)S(1)}, u32[]{:S(2)}, u32[]{:S(2)}) collective-permute-start(f32[40,128]{1,0:T(8,128)S(1)} %add_add_fusion.refs_1_), channel_id=1, source_target_pairs={{0,8},{8,0},{16,24},{24,16},{1,9},{9,1},{17,25},{25,17},{2,10},{10... | collective-permute-start | bytes 61448 | tf_op jit(solution)/shard_map/ppermute | solution.py:39
  (8 other events, 21.2 us)

commit v23 on v21

--- a/solution.py
+++ b/solution.py
@@ -418,8 +418,9 @@
             near, *passed = lax.optimization_barrier((near, *held[1:], *first))
             held[1:] = passed[: len(held) - 1]
             held += [near, trade(jnp.concatenate([rounded[group - late :], *held[1:]]), "row", d)]
-        chips = [rounded, *exchange([rounded] * (chips_n - 1), "col", 2)[::-1]]
-        return held, chips + [trade(chip, "col", 1) for chip in chips]
+        sent, other = lax.optimization_barrier((rounded, trade(rounded, "col", 1)))
+        chips = [rounded, *exchange([sent] * (chips_n - 1), "col", 2)[::-1]]
+        return held, [*chips, other, *(trade(chip, "col", 1) for chip in chips[1:])]
 
     def apply(rounded, table, degree, first=()):
         height = vectors_n + (DEGREE_ROWS if degree else 0)

time: 99.3 us -> 103 us (1.037)
  waiting for transfers between devices: 27 us -> 30.4 us
    ppermute x51, waiting for transfers between devices: 27 us -> 30.4 us  [trade(): return lax.ppermute(part, axis, [(i, i ^ d) for i in range(n)])]
  transfers between devices with their start and end apart: 51 -> 51, of which waited for: 25 -> 24; matrix products, arithmetic and copies ran while one was open for 0% -> 0% of each run, Pallas kernels for 5% -> 4%
where the time goes in v23:
time: 103 us
  starting transfers between devices  54.9 us (53%)
  waiting for transfers between devices  30.4 us (30%)
  Pallas kernels  12.9 us (13%)
  local copies, waits for them, and re-layouts  3.59 us (3%)
    ppermute x51, starting transfers between devices, trade(): return lax.ppermute(part, axis, [(i, i ^ d) for i in range(n)])  54.9 us
    ppermute x51, waiting for transfers between devices, trade(): return lax.ppermute(part, axis, [(i, i ^ d) for i in range(n)])  30.4 us
    pallas_call x17, Pallas kernels, call(): pl.pallas_call(lambda *refs: kernel(*refs[len(after):]), out_shape=jax.tr...  12.9 us
    unnamed x10, local copies, waits for them, and re-layouts  3.49 us
  transfers between devices with their start and end apart: 51, of which 24 were waited for; matrix products, arithmetic and copies ran while one was open for 0% of the time, Pallas kernels for 4%

profile of v23, /device:TPU:0, one launch (start us, length us, event | category | flops | bytes accessed | tf_op | source)
XLA Modules:
  0.0 102.8 jit_solution(1929898281454892848)
XLA Ops:
  0.6 0.9 copy-done
  2.1 3.7 %collective-permute-start.8 = (bf16[8,64,128]{2,1,0:T(8,128)(2,1)S(1)}, bf16[8,64,128]{2,1,0:T(8,128)(2,1)S(1)}, u32[]{:S(2)}, u32[]{:S(2)}) collective-permute-start(bf16[8,64,128]{2,1,0:T(8,128)(2,1)S(1)} %shard_map.61.refs_2_.refs_3_), channel_id=1, source_target_pairs={{0,16},{8,24},{16,0},{24,8},{1,17},{9,25},{17,1},{25,9},{2,18},{10... | collective-permute-start | bytes 393224 | tf_op jit(solution)/shard_map/ppermute | solution.py:39
  5.8 1.6 %collective-permute-start.7 = (bf16[7,64,128]{2,1,0:T(8,128)(2,1)S(1)}, bf16[7,64,128]{2,1,0:T(8,128)(2,1)S(1)}, u32[]{:S(2)}, u32[]{:S(2)}) collective-permute-start(bf16[7,64,128]{2,1,0:T(8,128)(2,1)S(1)} %slice.24), channel_id=1, source_target_pairs={{0,8},{8,0},{16,24},{24,16},{1,9},{9,1},{17,25},{25,17},{2,10},{10... | collective-permute-start | bytes 344072 | tf_op jit(solution)/shard_map/ppermute | solution.py:39
  7.4 2.4 %collective-permute-start.1 = (bf16[8,64,128]{2,1,0:T(8,128)(2,1)S(1)}, bf16[8,64,128]{2,1,0:T(8,128)(2,1)S(1)}, u32[]{:S(2)}, u32[]{:S(2)}) collective-permute-start(bf16[8,64,128]{2,1,0:T(8,128)(2,1)S(1)} %shard_map.61.refs_2_.refs_3_), channel_id=1, source_target_pairs={{0,6},{1,7},{2,4},{3,5},{4,2},{5,3},{6,0},{7,1},{8,14},{9,15},{10,... | collective-permute-start | bytes 393224 | tf_op jit(solution)/shard_map/ppermute | solution.py:39
  12.7 1.5 %collective-permute-start.9 = (bf16[9,64,128]{2,1,0:T(8,128)(2,1)S(1)}, bf16[9,64,128]{2,1,0:T(8,128)(2,1)S(1)}, u32[]{:S(2)}, u32[]{:S(2)}) collective-permute-start(bf16[9,64,128]{2,1,0:T(8,128)(2,1)S(1)} %pad_maximum_fusion), channel_id=1, source_target_pairs={{0,8},{8,0},{16,24},{24,16},{1,9},{9,1},{17,25},{25,17},{2,10},{10... | collective-permute-start | bytes 442376 | tf_op jit(solution)/shard_map/ppermute | solution.py:39
  14.2 2.2 %collective-permute-done.2.refs_4_ = bf16[8,64,128]{2,1,0:T(8,128)(2,1)S(1)} collective-permute-done((bf16[8,64,128]{2,1,0:T(8,128)(2,1)S(1)}, bf16[8,64,128]{2,1,0:T(8,128)(2,1)S(1)}, u32[]{:S(2)}, u32[]{:S(2)}) %collective-permute-start.2) | collective-permute-done | bytes 131104 | tf_op jit(solution)/shard_map/ppermute | solution.py:39
  17.0 1.2 %copy-done.2 = bf16[1,1,32,128,128]{4,3,2,1,0:T(8,128)(2,1)S(1)} copy-done((bf16[1,1,32,128,128]{4,3,2,1,0:T(8,128)(2,1)S(1)}, bf16[1,1,32,128,128]{4,3,2,1,0:T(8,128)(2,1)}, u32[]{:S(2)}) %copy-start.2) | copy-done | bytes 1048600
  18.3 1.2 %shard_map.63 = (f32[8,80,128]{2,1,0:T(8,128)S(1)}, f32[32,80,128]{2,1,0:T(8,128)S(1)}, bf16[528,128]{1,0:T(8,128)(2,1)S(1)}, bf16[528,128]{1,0:T(8,128)(2,1)S(1)}, bf16[528,128]{1,0:T(8,128)(2,1)S(1)}) custom-call(s32[3,32]{1,0:T(4,128)S(1)} %shard_map.59.refs_0_.refs_1_, ...), custom_call_target="tpu_custom_call", output_to_operand_aliasing={{1}: (10, {})} | custom-call | flops 67108864 | bytes 3408256 | tf_op jit(solution)/shard_map/pallas_call | solution.py:25
  19.5 1.5 %shard_map.64 = (f32[64,80,128]{2,1,0:T(8,128)S(1)}, bf16[4,528,128]{2,1,0:T(8,128)(2,1)S(1)}) custom-call(f32[8,80,128]{2,1,0:T(8,128)S(1)} %get-tuple-element.47.refs_0_.refs_3_, s32[3,32]{1,0:T(4,128)S(1)} %shard_map.59.refs_0_.refs_1_, bf16[32,128,128]{2,1,0:T(8,128)(2,1)S(1)} %shard_map.60.refs_1_.refs_2_, ...), custom_call_target="tpu_custom_call", output_to_operand_aliasing={{0}: (7, {})} | custom-call | flops 67108864 | bytes 4194688 | tf_op jit(solution)/shard_map/pallas_call | solution.py:25
  21.5 2.8 %collective-permute-start.15 = (bf16[528,128]{1,0:T(8,128)(2,1)S(1)}, bf16[528,128]{1,0:T(8,128)(2,1)S(1)}, u32[]{:S(2)}, u32[]{:S(2)}) collective-permute-start(bf16[528,128]{1,0:T(8,128)(2,1)S(1)} %get-tuple-element.59), channel_id=1, source_target_pairs={{0,16},{8,24},{16,0},{24,8},{1,17},{9,25},{17,1},{25,9},{2,18},{10... | collective-permute-start | bytes 405512 | tf_op jit(solution)/shard_map/ppermute | solution.py:39
  24.4 1.1 %collective-permute-start.16 = (bf16[528,128]{1,0:T(8,128)(2,1)S(1)}, bf16[528,128]{1,0:T(8,128)(2,1)S(1)}, u32[]{:S(2)}, u32[]{:S(2)}) collective-permute-start(bf16[528,128]{1,0:T(8,128)(2,1)S(1)} %get-tuple-element.60), channel_id=1, source_target_pairs={{0,24},{8,16},{16,8},{24,0},{1,25},{9,17},{17,9},{25,1},{2,26},{10... | collective-permute-start | bytes 405512 | tf_op jit(solution)/shard_map/ppermute | solution.py:39
  25.6 1.8 %collective-permute-start.11 = (bf16[528,128]{1,0:T(8,128)(2,1)S(1)}, bf16[528,128]{1,0:T(8,128)(2,1)S(1)}, u32[]{:S(2)}, u32[]{:S(2)}) collective-permute-start(bf16[528,128]{1,0:T(8,128)(2,1)S(1)} %get-tuple-element.55), channel_id=1, source_target_pairs={{0,6},{1,7},{2,4},{3,5},{4,2},{5,3},{6,0},{7,1},{8,14},{9,15},{10,... | collective-permute-start | bytes 405512 | tf_op jit(solution)/shard_map/ppermute | solution.py:39
  27.4 1.2 %collective-permute-start.12 = (bf16[528,128]{1,0:T(8,128)(2,1)S(1)}, bf16[528,128]{1,0:T(8,128)(2,1)S(1)}, u32[]{:S(2)}, u32[]{:S(2)}) collective-permute-start(bf16[528,128]{1,0:T(8,128)(2,1)S(1)} %get-tuple-element.56), channel_id=1, source_target_pairs={{0,4},{1,5},{2,6},{3,7},{4,0},{5,1},{6,2},{7,3},{8,12},{9,13},{10,... | collective-permute-start | bytes 405512 | tf_op jit(solution)/shard_map/ppermute | solution.py:39
  28.7 0.9 collective-permute-done.14.refs_7_
  29.5 1.5 %collective-permute-start.13 = (bf16[528,128]{1,0:T(8,128)(2,1)S(1)}, bf16[528,128]{1,0:T(8,128)(2,1)S(1)}, u32[]{:S(2)}, u32[]{:S(2)}) collective-permute-start(bf16[528,128]{1,0:T(8,128)(2,1)S(1)} %get-tuple-element.57), channel_id=1, source_target_pairs={{0,2},{1,3},{2,0},{3,1},{4,6},{5,7},{6,4},{7,5},{8,10},{9,11},{10,... | collective-permute-start | bytes 405512 | tf_op jit(solution)/shard_map/ppermute | solution.py:39
  31.0 3.7 %collective-permute-done.15.refs_8_ = bf16[528,128]{1,0:T(8,128)(2,1)S(1)} collective-permute-done((bf16[528,128]{1,0:T(8,128)(2,1)S(1)}, bf16[528,128]{1,0:T(8,128)(2,1)S(1)}, u32[]{:S(2)}, u32[]{:S(2)}) %collective-permute-start.15) | collective-permute-done | bytes 135200 | tf_op jit(solution)/shard_map/ppermute | solution.py:39
  35.0 3.8 %collective-permute-start.25 = (bf16[8,64,128]{2,1,0:T(8,128)(2,1)S(1)}, bf16[8,64,128]{2,1,0:T(8,128)(2,1)S(1)}, u32[]{:S(2)}, u32[]{:S(2)}) collective-permute-start(bf16[8,64,128]{2,1,0:T(8,128)(2,1)S(1)} %get-tuple-element.64.refs_2_.refs_3_), channel_id=1, source_target_pairs={{0,16},{8,24},{16,0},{24,8},{1,17},{9,25},{17,1},{25,9},{2,18},{10... | collective-permute-start | bytes 393224 | tf_op jit(solution)/shard_map/ppermute | solution.py:39
  38.9 2.5 %collective-permute-start.18 = (bf16[8,64,128]{2,1,0:T(8,128)(2,1)S(1)}, bf16[8,64,128]{2,1,0:T(8,128)(2,1)S(1)}, u32[]{:S(2)}, u32[]{:S(2)}) collective-permute-start(bf16[8,64,128]{2,1,0:T(8,128)(2,1)S(1)} %get-tuple-element.64.refs_2_.refs_3_), channel_id=1, source_target_pairs={{0,6},{1,7},{2,4},{3,5},{4,2},{5,3},{6,0},{7,1},{8,14},{9,15},{10,... | collective-permute-start | bytes 393224 | tf_op jit(solution)/shard_map/ppermute | solution.py:39
  42.7 2.0 %collective-permute-done.24.refs_5_ = bf16[7,64,128]{2,1,0:T(8,128)(2,1)S(1)} collective-permute-done((bf16[7,64,128]{2,1,0:T(8,128)(2,1)S(1)}, bf16[7,64,128]{2,1,0:T(8,128)(2,1)S(1)}, u32[]{:S(2)}, u32[]{:S(2)}) %collective-permute-start.24) | collective-permute-done | bytes 114720 | tf_op jit(solution)/shard_map/ppermute | solution.py:39
  44.7 1.0 collective-permute-done.25.refs_4_
  45.7 1.5 %collective-permute-start.26 = (bf16[9,64,128]{2,1,0:T(8,128)(2,1)S(1)}, bf16[9,64,128]{2,1,0:T(8,128)(2,1)S(1)}, u32[]{:S(2)}, u32[]{:S(2)}) collective-permute-start(bf16[9,64,128]{2,1,0:T(8,128)(2,1)S(1)} %pad_maximum_fusion.1), channel_id=1, source_target_pairs={{0,8},{8,0},{16,24},{24,16},{1,9},{9,1},{17,25},{25,17},{2,10},{10... | collective-permute-start | bytes 442376 | tf_op jit(solution)/shard_map/ppermute | solution.py:39
  47.3 1.0 collective-permute-done.19.refs_4_
  48.8 0.8 collective-permute-done.22.refs_8_
  49.8 1.0 %shard_map.68 = (f32[8,64,128]{2,1,0:T(8,128)S(1)}, f32[32,64,128]{2,1,0:T(8,128)S(1)}, bf16[512,128]{1,0:T(8,128)(2,1)S(1)}, bf16[512,128]{1,0:T(8,128)(2,1)S(1)}, bf16[512,128]{1,0:T(8,128)(2,1)S(1)}) custom-call(s32[3,32]{1,0:T(4,128)S(1)} %shard_map.59.refs_0_.refs_1_, ...), custom_call_target="tpu_custom_call", output_to_operand_aliasing={{1}: (10, {})} | custom-call | flops 67108864 | bytes 3146112 | tf_op jit(solution)/shard_map/pallas_call | solution.py:25
  51.4 1.4 %shard_map.69 = (f32[64,64,128]{2,1,0:T(8,128)S(1)}, bf16[4,512,128]{2,1,0:T(8,128)(2,1)S(1)}) custom-call(f32[8,64,128]{2,1,0:T(8,128)S(1)} %get-tuple-element.67.refs_0_.refs_4_, s32[3,32]{1,0:T(4,128)S(1)} %shard_map.59.refs_0_.refs_1_, bf16[32,128,128]{2,1,0:T(8,128)(2,1)S(1)} %shard_map.60.refs_1_.refs_2_, ...), custom_call_target="tpu_custom_call", output_to_operand_aliasing={{0}: (7, {})} | custom-call | flops 67108864 | bytes 3670400 | tf_op jit(solution)/shard_map/pallas_call | solution.py:25
  52.9 1.4 %collective-permute-start.31 = (bf16[512,128]{1,0:T(8,128)(2,1)S(1)}, bf16[512,128]{1,0:T(8,128)(2,1)S(1)}, u32[]{:S(2)}, u32[]{:S(2)}) collective-permute-start(bf16[512,128]{1,0:T(8,128)(2,1)S(1)} %get-tuple-element.77), channel_id=1, source_target_pairs={{0,8},{8,0},{16,24},{24,16},{1,9},{9,1},{17,25},{25,17},{2,10},{10... | collective-permute-start | bytes 393224 | tf_op jit(solution)/shard_map/ppermute | solution.py:39
  54.7 2.7 %collective-permute-start.33 = (bf16[512,128]{1,0:T(8,128)(2,1)S(1)}, bf16[512,128]{1,0:T(8,128)(2,1)S(1)}, u32[]{:S(2)}, u32[]{:S(2)}) collective-permute-start(bf16[512,128]{1,0:T(8,128)(2,1)S(1)} %get-tuple-element.79), channel_id=1, source_target_pairs={{0,24},{8,16},{16,8},{24,0},{1,25},{9,17},{17,9},{25,1},{2,26},{10... | collective-permute-start | bytes 393224 | tf_op jit(solution)/shard_map/ppermute | solution.py:39
  57.5 2.5 %collective-permute-start.28 = (bf16[512,128]{1,0:T(8,128)(2,1)S(1)}, bf16[512,128]{1,0:T(8,128)(2,1)S(1)}, u32[]{:S(2)}, u32[]{:S(2)}) collective-permute-start(bf16[512,128]{1,0:T(8,128)(2,1)S(1)} %get-tuple-element.74), channel_id=1, source_target_pairs={{0,6},{1,7},{2,4},{3,5},{4,2},{5,3},{6,0},{7,1},{8,14},{9,15},{10,... | collective-permute-start | bytes 393224 | tf_op jit(solution)/shard_map/ppermute | solution.py:39
  60.5 1.5 %collective-permute-start.30 = (bf16[512,128]{1,0:T(8,128)(2,1)S(1)}, bf16[512,128]{1,0:T(8,128)(2,1)S(1)}, u32[]{:S(2)}, u32[]{:S(2)}) collective-permute-start(bf16[512,128]{1,0:T(8,128)(2,1)S(1)} %get-tuple-element.76), channel_id=1, source_target_pairs={{0,2},{1,3},{2,0},{3,1},{4,6},{5,7},{6,4},{7,5},{8,10},{9,11},{10,... | collective-permute-start | bytes 393224 | tf_op jit(solution)/shard_map/ppermute | solution.py:39
  62.0 5.3 %collective-permute-done.32.refs_9_ = bf16[512,128]{1,0:T(8,128)(2,1)S(1)} collective-permute-done((bf16[512,128]{1,0:T(8,128)(2,1)S(1)}, bf16[512,128]{1,0:T(8,128)(2,1)S(1)}, u32[]{:S(2)}, u32[]{:S(2)}) %collective-permute-start.32) | collective-permute-done | bytes 131104 | tf_op jit(solution)/shard_map/ppermute | solution.py:39
  67.6 2.5 %collective-permute-start.42 = (bf16[8,64,128]{2,1,0:T(8,128)(2,1)S(1)}, bf16[8,64,128]{2,1,0:T(8,128)(2,1)S(1)}, u32[]{:S(2)}, u32[]{:S(2)}) collective-permute-start(bf16[8,64,128]{2,1,0:T(8,128)(2,1)S(1)} %get-tuple-element.82.refs_2_.refs_3_), channel_id=1, source_target_pairs={{0,16},{8,24},{16,0},{24,8},{1,17},{9,25},{17,1},{25,9},{2,18},{10... | collective-permute-start | bytes 393224 | tf_op jit(solution)/shard_map/ppermute | solution.py:39
  70.2 2.5 %collective-permute-start.35 = (bf16[8,64,128]{2,1,0:T(8,128)(2,1)S(1)}, bf16[8,64,128]{2,1,0:T(8,128)(2,1)S(1)}, u32[]{:S(2)}, u32[]{:S(2)}) collective-permute-start(bf16[8,64,128]{2,1,0:T(8,128)(2,1)S(1)} %get-tuple-element.82.refs_2_.refs_3_), channel_id=1, source_target_pairs={{0,6},{1,7},{2,4},{3,5},{4,2},{5,3},{6,0},{7,1},{8,14},{9,15},{10,... | collective-permute-start | bytes 393224 | tf_op jit(solution)/shard_map/ppermute | solution.py:39
  74.4 1.7 %collective-permute-done.41.refs_5_ = bf16[7,64,128]{2,1,0:T(8,128)(2,1)S(1)} collective-permute-done((bf16[7,64,128]{2,1,0:T(8,128)(2,1)S(1)}, bf16[7,64,128]{2,1,0:T(8,128)(2,1)S(1)}, u32[]{:S(2)}, u32[]{:S(2)}) %collective-permute-start.41) | collective-permute-done | bytes 114720 | tf_op jit(solution)/shard_map/ppermute | solution.py:39
  76.1 1.1 %collective-permute-done.42.refs_4_ = bf16[8,64,128]{2,1,0:T(8,128)(2,1)S(1)} collective-permute-done((bf16[8,64,128]{2,1,0:T(8,128)(2,1)S(1)}, bf16[8,64,128]{2,1,0:T(8,128)(2,1)S(1)}, u32[]{:S(2)}, u32[]{:S(2)}) %collective-permute-start.42) | collective-permute-done | bytes 131104 | tf_op jit(solution)/shard_map/ppermute | solution.py:39
  77.2 1.3 %collective-permute-start.43 = (bf16[9,64,128]{2,1,0:T(8,128)(2,1)S(1)}, bf16[9,64,128]{2,1,0:T(8,128)(2,1)S(1)}, u32[]{:S(2)}, u32[]{:S(2)}) collective-permute-start(bf16[9,64,128]{2,1,0:T(8,128)(2,1)S(1)} %pad_maximum_fusion.2), channel_id=1, source_target_pairs={{0,8},{8,0},{16,24},{24,16},{1,9},{9,1},{17,25},{25,17},{2,10},{10... | collective-permute-start | bytes 442376 | tf_op jit(solution)/shard_map/ppermute | solution.py:39
  78.6 1.0 collective-permute-done.36.refs_4_
  80.1 0.8 collective-permute-done.39.refs_8_
  81.1 1.0 shard_map.72.refs_1_
  82.7 1.2 %shard_map.74 = f32[40,128]{1,0:T(8,128)S(1)} custom-call(s32[3,32]{1,0:T(4,128)S(1)} %shard_map.59.refs_0_.refs_1_, bf16[64,4096]{1,0:T(8,128)(2,1)S(1)} %shard_map.72.refs_1_, f32[64,128]{1,0:T(8,128)S(1)} %shard_map.73.refs_2_, bf16[8,64,128]{2,1,0:T(8,128)(2,1)S(1)} %get-tuple-element.82.refs_2_.refs_3_, ...), custom_call_target="tpu_custom_call" | custom-call | flops 33554432 | bytes 1081728 | tf_op jit(solution)/shard_map/pallas_call | solution.py:25
  84.0 1.2 %collective-permute-done.44 = f32[40,128]{1,0:T(8,128)S(1)} collective-permute-done((f32[40,128]{1,0:T(8,128)S(1)}, f32[40,128]{1,0:T(8,128)S(1)}, u32[]{:S(2)}, u32[]{:S(2)}) %collective-permute-start.44) | collective-permute-done | bytes 20512 | tf_op jit(solution)/shard_map/ppermute | solution.py:39
  85.1 2.2 %collective-permute-start.45 = (f32[40,128]{1,0:T(8,128)S(1)}, f32[40,128]{1,0:T(8,128)S(1)}, u32[]{:S(2)}, u32[]{:S(2)}) collective-permute-start(f32[40,128]{1,0:T(8,128)S(1)} %add.12), channel_id=1, source_target_pairs={{0,6},{1,7},{2,4},{3,5},{4,2},{5,3},{6,0},{7,1},{8,14},{9,15},{10,... | collective-permute-start | bytes 61448 | tf_op jit(solution)/shard_map/ppermute | solution.py:39
  88.6 1.2 %collective-permute-done.45 = f32[40,128]{1,0:T(8,128)S(1)} collective-permute-done((f32[40,128]{1,0:T(8,128)S(1)}, f32[40,128]{1,0:T(8,128)S(1)}, u32[]{:S(2)}, u32[]{:S(2)}) %collective-permute-start.45) | collective-permute-done | bytes 20512 | tf_op jit(solution)/shard_map/ppermute | solution.py:39
  89.8 1.3 %collective-permute-done.46 = f32[40,128]{1,0:T(8,128)S(1)} collective-permute-done((f32[40,128]{1,0:T(8,128)S(1)}, f32[40,128]{1,0:T(8,128)S(1)}, u32[]{:S(2)}, u32[]{:S(2)}) %collective-permute-start.46) | collective-permute-done | bytes 20512 | tf_op jit(solution)/shard_map/ppermute | solution.py:39
  91.9 2.5 %collective-permute-start.48 = (f32[40,128]{1,0:T(8,128)S(1)}, f32[40,128]{1,0:T(8,128)S(1)}, u32[]{:S(2)}, u32[]{:S(2)}) collective-permute-start(f32[40,128]{1,0:T(8,128)S(1)} %add_add_fusion.refs_1_), channel_id=1, source_target_pairs={{0,24},{8,16},{16,8},{24,0},{1,25},{9,17},{17,9},{25,1},{2,26},{10... | collective-permute-start | bytes 61448 | tf_op jit(solution)/shard_map/ppermute | solution.py:39
  94.7 1.6 %collective-permute-start.50 = (f32[40,128]{1,0:T(8,128)S(1)}, f32[40,128]{1,0:T(8,128)S(1)}, u32[]{:S(2)}, u32[]{:S(2)}) collective-permute-start(f32[40,128]{1,0:T(8,128)S(1)} %add_add_fusion.refs_1_), channel_id=1, source_target_pairs={{0,8},{8,0},{16,24},{24,16},{1,9},{9,1},{17,25},{25,17},{2,10},{10... | collective-permute-start | bytes 61448 | tf_op jit(solution)/shard_map/ppermute | solution.py:39
  96.3 1.3 %collective-permute-done.48.refs_2_ = f32[40,128]{1,0:T(8,128)S(1)} collective-permute-done((f32[40,128]{1,0:T(8,128)S(1)}, f32[40,128]{1,0:T(8,128)S(1)}, u32[]{:S(2)}, u32[]{:S(2)}) %collective-permute-start.48) | collective-permute-done | bytes 20512 | tf_op jit(solution)/shard_map/ppermute | solution.py:39
  97.6 1.4 %collective-permute-done.49.refs_3_ = f32[40,128]{1,0:T(8,128)S(1)} collective-permute-done((f32[40,128]{1,0:T(8,128)S(1)}, f32[40,128]{1,0:T(8,128)S(1)}, u32[]{:S(2)}, u32[]{:S(2)}) %collective-permute-start.49) | collective-permute-done | bytes 20512 | tf_op jit(solution)/shard_map/ppermute | solution.py:39
  99.1 3.8 %shard_map.75 = (f32[64,1024]{1,0:T(8,128)}, f32[64,64]{1,0:T(8,128)}) custom-call(f32[64,1024]{1,0:T(8,128)S(1)} %get-tuple-element.80.refs_0_, f32[40,128]{1,0:T(8,128)S(1)} %add_add_fusion.refs_1_, f32[40,128]{1,0:T(8,128)S(1)} %collective-permute-done.48.refs_2_, f32[40,128]{1,0:T(8,128)S(1)} %collective-permute-done.49.refs_3_, ...), custom_call_target="tpu_custom_call" | custom-call | bytes 344064 | tf_op jit(solution)/shard_map/pallas_call | solution.py:25
  (94 shorter events, 14.4 us)
Async XLA Ops:
  1.6 5.8 %collective-permute-start = (bf16[8,64,128]{2,1,0:T(8,128)(2,1)S(1)}, bf16[8,64,128]{2,1,0:T(8,128)(2,1)S(1)}, u32[]{:S(2)}, u32[]{:S(2)}) collective-permute-start(bf16[8,64,128]{2,1,0:T(8,128)(2,1)S(1)} %shard_map.61.refs_2_.refs_3_), channel_id=1, source_target_pairs={{0,1},{1,0},{2,3},{3,2},{4,5},{5,4},{6,7},{7,6},{8,9},{9,8},{10,11... | collective-permute-start | bytes 393224 | tf_op jit(solution)/shard_map/ppermute | solution.py:39
  2.1 10.6 %collective-permute-start.8 = (bf16[8,64,128]{2,1,0:T(8,128)(2,1)S(1)}, bf16[8,64,128]{2,1,0:T(8,128)(2,1)S(1)}, u32[]{:S(2)}, u32[]{:S(2)}) collective-permute-start(bf16[8,64,128]{2,1,0:T(8,128)(2,1)S(1)} %shard_map.61.refs_2_.refs_3_), channel_id=1, source_target_pairs={{0,16},{8,24},{16,0},{24,8},{1,17},{9,25},{17,1},{25,9},{2,18},{10... | collective-permute-start | bytes 393224 | tf_op jit(solution)/shard_map/ppermute | solution.py:39
  5.8 6.9 %collective-permute-start.7 = (bf16[7,64,128]{2,1,0:T(8,128)(2,1)S(1)}, bf16[7,64,128]{2,1,0:T(8,128)(2,1)S(1)}, u32[]{:S(2)}, u32[]{:S(2)}) collective-permute-start(bf16[7,64,128]{2,1,0:T(8,128)(2,1)S(1)} %slice.24), channel_id=1, source_target_pairs={{0,8},{8,0},{16,24},{24,16},{1,9},{9,1},{17,25},{25,17},{2,10},{10... | collective-permute-start | bytes 344072 | tf_op jit(solution)/shard_map/ppermute | solution.py:39
  7.4 6.8 %collective-permute-start.1 = (bf16[8,64,128]{2,1,0:T(8,128)(2,1)S(1)}, bf16[8,64,128]{2,1,0:T(8,128)(2,1)S(1)}, u32[]{:S(2)}, u32[]{:S(2)}) collective-permute-start(bf16[8,64,128]{2,1,0:T(8,128)(2,1)S(1)} %shard_map.61.refs_2_.refs_3_), channel_id=1, source_target_pairs={{0,6},{1,7},{2,4},{3,5},{4,2},{5,3},{6,0},{7,1},{8,14},{9,15},{10,... | collective-permute-start | bytes 393224 | tf_op jit(solution)/shard_map/ppermute | solution.py:39
  9.9 6.5 %collective-permute-start.2 = (bf16[8,64,128]{2,1,0:T(8,128)(2,1)S(1)}, bf16[8,64,128]{2,1,0:T(8,128)(2,1)S(1)}, u32[]{:S(2)}, u32[]{:S(2)}) collective-permute-start(bf16[8,64,128]{2,1,0:T(8,128)(2,1)S(1)} %shard_map.61.refs_2_.refs_3_), channel_id=1, source_target_pairs={{0,4},{1,5},{2,6},{3,7},{4,0},{5,1},{6,2},{7,3},{8,12},{9,13},{10,... | collective-permute-start | bytes 393224 | tf_op jit(solution)/shard_map/ppermute | solution.py:39
  10.4 6.1 %collective-permute-start.3 = (bf16[8,64,128]{2,1,0:T(8,128)(2,1)S(1)}, bf16[8,64,128]{2,1,0:T(8,128)(2,1)S(1)}, u32[]{:S(2)}, u32[]{:S(2)}) collective-permute-start(bf16[8,64,128]{2,1,0:T(8,128)(2,1)S(1)} %shard_map.61.refs_2_.refs_3_), channel_id=1, source_target_pairs={{0,2},{1,3},{2,0},{3,1},{4,6},{5,7},{6,4},{7,5},{8,10},{9,11},{10,... | collective-permute-start | bytes 393224 | tf_op jit(solution)/shard_map/ppermute | solution.py:39
  12.7 6.7 %collective-permute-start.9 = (bf16[9,64,128]{2,1,0:T(8,128)(2,1)S(1)}, bf16[9,64,128]{2,1,0:T(8,128)(2,1)S(1)}, u32[]{:S(2)}, u32[]{:S(2)}) collective-permute-start(bf16[9,64,128]{2,1,0:T(8,128)(2,1)S(1)} %pad_maximum_fusion), channel_id=1, source_target_pairs={{0,8},{8,0},{16,24},{24,16},{1,9},{9,1},{17,25},{25,17},{2,10},{10... | collective-permute-start | bytes 442376 | tf_op jit(solution)/shard_map/ppermute | solution.py:39
  14.2 4.0 %collective-permute-start.4 = (bf16[8,64,128]{2,1,0:T(8,128)(2,1)S(1)}, bf16[8,64,128]{2,1,0:T(8,128)(2,1)S(1)}, u32[]{:S(2)}, u32[]{:S(2)}) collective-permute-start(bf16[8,64,128]{2,1,0:T(8,128)(2,1)S(1)} %collective-permute-done.1.refs_3_), channel_id=1, source_target_pairs={{0,1},{1,0},{2,3},{3,2},{4,5},{5,4},{6,7},{7,6},{8,9},{9,8},{10,11... | collective-permute-start | bytes 393224 | tf_op jit(solution)/shard_map/ppermute | solution.py:39
  16.4 1.8 %collective-permute-start.5 = (bf16[8,64,128]{2,1,0:T(8,128)(2,1)S(1)}, bf16[8,64,128]{2,1,0:T(8,128)(2,1)S(1)}, u32[]{:S(2)}, u32[]{:S(2)}) collective-permute-start(bf16[8,64,128]{2,1,0:T(8,128)(2,1)S(1)} %collective-permute-done.2.refs_4_), channel_id=1, source_target_pairs={{0,1},{1,0},{2,3},{3,2},{4,5},{5,4},{6,7},{7,6},{8,9},{9,8},{10,11... | collective-permute-start | bytes 393224 | tf_op jit(solution)/shard_map/ppermute | solution.py:39
  16.5 1.8 %collective-permute-start.6 = (bf16[8,64,128]{2,1,0:T(8,128)(2,1)S(1)}, bf16[8,64,128]{2,1,0:T(8,128)(2,1)S(1)}, u32[]{:S(2)}, u32[]{:S(2)}) collective-permute-start(bf16[8,64,128]{2,1,0:T(8,128)(2,1)S(1)} %collective-permute-done.3.refs_5_), channel_id=1, source_target_pairs={{0,1},{1,0},{2,3},{3,2},{4,5},{5,4},{6,7},{7,6},{8,9},{9,8},{10,11... | collective-permute-start | bytes 393224 | tf_op jit(solution)/shard_map/ppermute | solution.py:39
  21.0 4.5 %collective-permute-start.10 = (bf16[4,528,128]{2,1,0:T(8,128)(2,1)S(1)}, bf16[4,528,128]{2,1,0:T(8,128)(2,1)S(1)}, u32[]{:S(2)}, u32[]{:S(2)}) collective-permute-start(bf16[4,528,128]{2,1,0:T(8,128)(2,1)S(1)} %get-tuple-element.52), channel_id=1, source_target_pairs={{0,1},{1,0},{2,3},{3,2},{4,5},{5,4},{6,7},{7,6},{8,9},{9,8},{10,11... | collective-permute-start | bytes 1622024 | tf_op jit(solution)/shard_map/ppermute | solution.py:39
  21.1 8.5 %collective-permute-start.14 = (bf16[528,128]{1,0:T(8,128)(2,1)S(1)}, bf16[528,128]{1,0:T(8,128)(2,1)S(1)}, u32[]{:S(2)}, u32[]{:S(2)}) collective-permute-start(bf16[528,128]{1,0:T(8,128)(2,1)S(1)} %get-tuple-element.58), channel_id=1, source_target_pairs={{0,8},{8,0},{16,24},{24,16},{1,9},{9,1},{17,25},{25,17},{2,10},{10... | collective-permute-start | bytes 405512 | tf_op jit(solution)/shard_map/ppermute | solution.py:39
  21.5 13.1 %collective-permute-start.15 = (bf16[528,128]{1,0:T(8,128)(2,1)S(1)}, bf16[528,128]{1,0:T(8,128)(2,1)S(1)}, u32[]{:S(2)}, u32[]{:S(2)}) collective-permute-start(bf16[528,128]{1,0:T(8,128)(2,1)S(1)} %get-tuple-element.59), channel_id=1, source_target_pairs={{0,16},{8,24},{16,0},{24,8},{1,17},{9,25},{17,1},{25,9},{2,18},{10... | collective-permute-start | bytes 405512 | tf_op jit(solution)/shard_map/ppermute | solution.py:39
  24.4 10.3 %collective-permute-start.16 = (bf16[528,128]{1,0:T(8,128)(2,1)S(1)}, bf16[528,128]{1,0:T(8,128)(2,1)S(1)}, u32[]{:S(2)}, u32[]{:S(2)}) collective-permute-start(bf16[528,128]{1,0:T(8,128)(2,1)S(1)} %get-tuple-element.60), channel_id=1, source_target_pairs={{0,24},{8,16},{16,8},{24,0},{1,25},{9,17},{17,9},{25,1},{2,26},{10... | collective-permute-start | bytes 405512 | tf_op jit(solution)/shard_map/ppermute | solution.py:39
  25.6 9.1 %collective-permute-start.11 = (bf16[528,128]{1,0:T(8,128)(2,1)S(1)}, bf16[528,128]{1,0:T(8,128)(2,1)S(1)}, u32[]{:S(2)}, u32[]{:S(2)}) collective-permute-start(bf16[528,128]{1,0:T(8,128)(2,1)S(1)} %get-tuple-element.55), channel_id=1, source_target_pairs={{0,6},{1,7},{2,4},{3,5},{4,2},{5,3},{6,0},{7,1},{8,14},{9,15},{10,... | collective-permute-start | bytes 405512 | tf_op jit(solution)/shard_map/ppermute | solution.py:39
  27.4 7.3 %collective-permute-start.12 = (bf16[528,128]{1,0:T(8,128)(2,1)S(1)}, bf16[528,128]{1,0:T(8,128)(2,1)S(1)}, u32[]{:S(2)}, u32[]{:S(2)}) collective-permute-start(bf16[528,128]{1,0:T(8,128)(2,1)S(1)} %get-tuple-element.56), channel_id=1, source_target_pairs={{0,4},{1,5},{2,6},{3,7},{4,0},{5,1},{6,2},{7,3},{8,12},{9,13},{10,... | collective-permute-start | bytes 405512 | tf_op jit(solution)/shard_map/ppermute | solution.py:39
  29.5 5.2 %collective-permute-start.13 = (bf16[528,128]{1,0:T(8,128)(2,1)S(1)}, bf16[528,128]{1,0:T(8,128)(2,1)S(1)}, u32[]{:S(2)}, u32[]{:S(2)}) collective-permute-start(bf16[528,128]{1,0:T(8,128)(2,1)S(1)} %get-tuple-element.57), channel_id=1, source_target_pairs={{0,2},{1,3},{2,0},{3,1},{4,6},{5,7},{6,4},{7,5},{8,10},{9,11},{10,... | collective-permute-start | bytes 405512 | tf_op jit(solution)/shard_map/ppermute | solution.py:39
  34.9 4.0 %collective-permute-start.17 = (bf16[8,64,128]{2,1,0:T(8,128)(2,1)S(1)}, bf16[8,64,128]{2,1,0:T(8,128)(2,1)S(1)}, u32[]{:S(2)}, u32[]{:S(2)}) collective-permute-start(bf16[8,64,128]{2,1,0:T(8,128)(2,1)S(1)} %get-tuple-element.64.refs_2_.refs_3_), channel_id=1, source_target_pairs={{0,1},{1,0},{2,3},{3,2},{4,5},{5,4},{6,7},{7,6},{8,9},{9,8},{10,11... | collective-permute-start | bytes 393224 | tf_op jit(solution)/shard_map/ppermute | solution.py:39
  35.0 10.7 %collective-permute-start.25 = (bf16[8,64,128]{2,1,0:T(8,128)(2,1)S(1)}, bf16[8,64,128]{2,1,0:T(8,128)(2,1)S(1)}, u32[]{:S(2)}, u32[]{:S(2)}) collective-permute-start(bf16[8,64,128]{2,1,0:T(8,128)(2,1)S(1)} %get-tuple-element.64.refs_2_.refs_3_), channel_id=1, source_target_pairs={{0,16},{8,24},{16,0},{24,8},{1,17},{9,25},{17,1},{25,9},{2,18},{10... | collective-permute-start | bytes 393224 | tf_op jit(solution)/shard_map/ppermute | solution.py:39
  38.8 5.9 %collective-permute-start.24 = (bf16[7,64,128]{2,1,0:T(8,128)(2,1)S(1)}, bf16[7,64,128]{2,1,0:T(8,128)(2,1)S(1)}, u32[]{:S(2)}, u32[]{:S(2)}) collective-permute-start(bf16[7,64,128]{2,1,0:T(8,128)(2,1)S(1)} %slice.20), channel_id=1, source_target_pairs={{0,8},{8,0},{16,24},{24,16},{1,9},{9,1},{17,25},{25,17},{2,10},{10... | collective-permute-start | bytes 344072 | tf_op jit(solution)/shard_map/ppermute | solution.py:39
  38.9 8.3 %collective-permute-start.18 = (bf16[8,64,128]{2,1,0:T(8,128)(2,1)S(1)}, bf16[8,64,128]{2,1,0:T(8,128)(2,1)S(1)}, u32[]{:S(2)}, u32[]{:S(2)}) collective-permute-start(bf16[8,64,128]{2,1,0:T(8,128)(2,1)S(1)} %get-tuple-element.64.refs_2_.refs_3_), channel_id=1, source_target_pairs={{0,6},{1,7},{2,4},{3,5},{4,2},{5,3},{6,0},{7,1},{8,14},{9,15},{10,... | collective-permute-start | bytes 393224 | tf_op jit(solution)/shard_map/ppermute | solution.py:39
  41.4 6.8 %collective-permute-start.19 = (bf16[8,64,128]{2,1,0:T(8,128)(2,1)S(1)}, bf16[8,64,128]{2,1,0:T(8,128)(2,1)S(1)}, u32[]{:S(2)}, u32[]{:S(2)}) collective-permute-start(bf16[8,64,128]{2,1,0:T(8,128)(2,1)S(1)} %get-tuple-element.64.refs_2_.refs_3_), channel_id=1, source_target_pairs={{0,4},{1,5},{2,6},{3,7},{4,0},{5,1},{6,2},{7,3},{8,12},{9,13},{10,... | collective-permute-start | bytes 393224 | tf_op jit(solution)/shard_map/ppermute | solution.py:39
  42.0 6.4 %collective-permute-start.20 = (bf16[8,64,128]{2,1,0:T(8,128)(2,1)S(1)}, bf16[8,64,128]{2,1,0:T(8,128)(2,1)S(1)}, u32[]{:S(2)}, u32[]{:S(2)}) collective-permute-start(bf16[8,64,128]{2,1,0:T(8,128)(2,1)S(1)} %get-tuple-element.64.refs_2_.refs_3_), channel_id=1, source_target_pairs={{0,2},{1,3},{2,0},{3,1},{4,6},{5,7},{6,4},{7,5},{8,10},{9,11},{10,... | collective-permute-start | bytes 393224 | tf_op jit(solution)/shard_map/ppermute | solution.py:39
  45.7 5.7 %collective-permute-start.26 = (bf16[9,64,128]{2,1,0:T(8,128)(2,1)S(1)}, bf16[9,64,128]{2,1,0:T(8,128)(2,1)S(1)}, u32[]{:S(2)}, u32[]{:S(2)}) collective-permute-start(bf16[9,64,128]{2,1,0:T(8,128)(2,1)S(1)} %pad_maximum_fusion.1), channel_id=1, source_target_pairs={{0,8},{8,0},{16,24},{24,16},{1,9},{9,1},{17,25},{25,17},{2,10},{10... | collective-permute-start | bytes 442376 | tf_op jit(solution)/shard_map/ppermute | solution.py:39
  47.3 1.5 %collective-permute-start.21 = (bf16[8,64,128]{2,1,0:T(8,128)(2,1)S(1)}, bf16[8,64,128]{2,1,0:T(8,128)(2,1)S(1)}, u32[]{:S(2)}, u32[]{:S(2)}) collective-permute-start(bf16[8,64,128]{2,1,0:T(8,128)(2,1)S(1)} %collective-permute-done.18.refs_3_), channel_id=1, source_target_pairs={{0,1},{1,0},{2,3},{3,2},{4,5},{5,4},{6,7},{7,6},{8,9},{9,8},{10,11... | collective-permute-start | bytes 393224 | tf_op jit(solution)/shard_map/ppermute | solution.py:39
  48.4 1.4 %collective-permute-start.23 = (bf16[8,64,128]{2,1,0:T(8,128)(2,1)S(1)}, bf16[8,64,128]{2,1,0:T(8,128)(2,1)S(1)}, u32[]{:S(2)}, u32[]{:S(2)}) collective-permute-start(bf16[8,64,128]{2,1,0:T(8,128)(2,1)S(1)} %collective-permute-done.20.refs_5_), channel_id=1, source_target_pairs={{0,1},{1,0},{2,3},{3,2},{4,5},{5,4},{6,7},{7,6},{8,9},{9,8},{10,11... | collective-permute-start | bytes 393224 | tf_op jit(solution)/shard_map/ppermute | solution.py:39
  52.9 4.5 %collective-permute-start.27 = (bf16[4,512,128]{2,1,0:T(8,128)(2,1)S(1)}, bf16[4,512,128]{2,1,0:T(8,128)(2,1)S(1)}, u32[]{:S(2)}, u32[]{:S(2)}) collective-permute-start(bf16[4,512,128]{2,1,0:T(8,128)(2,1)S(1)} %get-tuple-element.72), channel_id=1, source_target_pairs={{0,1},{1,0},{2,3},{3,2},{4,5},{5,4},{6,7},{7,6},{8,9},{9,8},{10,11... | collective-permute-start | bytes 1572872 | tf_op jit(solution)/shard_map/ppermute | solution.py:39
  52.9 7.6 %collective-permute-start.31 = (bf16[512,128]{1,0:T(8,128)(2,1)S(1)}, bf16[512,128]{1,0:T(8,128)(2,1)S(1)}, u32[]{:S(2)}, u32[]{:S(2)}) collective-permute-start(bf16[512,128]{1,0:T(8,128)(2,1)S(1)} %get-tuple-element.77), channel_id=1, source_target_pairs={{0,8},{8,0},{16,24},{24,16},{1,9},{9,1},{17,25},{25,17},{2,10},{10... | collective-permute-start | bytes 393224 | tf_op jit(solution)/shard_map/ppermute | solution.py:39
  54.4 12.9 %collective-permute-start.32 = (bf16[512,128]{1,0:T(8,128)(2,1)S(1)}, bf16[512,128]{1,0:T(8,128)(2,1)S(1)}, u32[]{:S(2)}, u32[]{:S(2)}) collective-permute-start(bf16[512,128]{1,0:T(8,128)(2,1)S(1)} %get-tuple-element.78), channel_id=1, source_target_pairs={{0,16},{8,24},{16,0},{24,8},{1,17},{9,25},{17,1},{25,9},{2,18},{10... | collective-permute-start | bytes 393224 | tf_op jit(solution)/shard_map/ppermute | solution.py:39
  54.7 12.6 %collective-permute-start.33 = (bf16[512,128]{1,0:T(8,128)(2,1)S(1)}, bf16[512,128]{1,0:T(8,128)(2,1)S(1)}, u32[]{:S(2)}, u32[]{:S(2)}) collective-permute-start(bf16[512,128]{1,0:T(8,128)(2,1)S(1)} %get-tuple-element.79), channel_id=1, source_target_pairs={{0,24},{8,16},{16,8},{24,0},{1,25},{9,17},{17,9},{25,1},{2,26},{10... | collective-permute-start | bytes 393224 | tf_op jit(solution)/shard_map/ppermute | solution.py:39
  57.5 9.8 %collective-permute-start.28 = (bf16[512,128]{1,0:T(8,128)(2,1)S(1)}, bf16[512,128]{1,0:T(8,128)(2,1)S(1)}, u32[]{:S(2)}, u32[]{:S(2)}) collective-permute-start(bf16[512,128]{1,0:T(8,128)(2,1)S(1)} %get-tuple-element.74), channel_id=1, source_target_pairs={{0,6},{1,7},{2,4},{3,5},{4,2},{5,3},{6,0},{7,1},{8,14},{9,15},{10,... | collective-permute-start | bytes 393224 | tf_op jit(solution)/shard_map/ppermute | solution.py:39
  60.0 7.3 %collective-permute-start.29 = (bf16[512,128]{1,0:T(8,128)(2,1)S(1)}, bf16[512,128]{1,0:T(8,128)(2,1)S(1)}, u32[]{:S(2)}, u32[]{:S(2)}) collective-permute-start(bf16[512,128]{1,0:T(8,128)(2,1)S(1)} %get-tuple-element.75), channel_id=1, source_target_pairs={{0,4},{1,5},{2,6},{3,7},{4,0},{5,1},{6,2},{7,3},{8,12},{9,13},{10,... | collective-permute-start | bytes 393224 | tf_op jit(solution)/shard_map/ppermute | solution.py:39
  60.5 6.8 %collective-permute-start.30 = (bf16[512,128]{1,0:T(8,128)(2,1)S(1)}, bf16[512,128]{1,0:T(8,128)(2,1)S(1)}, u32[]{:S(2)}, u32[]{:S(2)}) collective-permute-start(bf16[512,128]{1,0:T(8,128)(2,1)S(1)} %get-tuple-element.76), channel_id=1, source_target_pairs={{0,2},{1,3},{2,0},{3,1},{4,6},{5,7},{6,4},{7,5},{8,10},{9,11},{10,... | collective-permute-start | bytes 393224 | tf_op jit(solution)/shard_map/ppermute | solution.py:39
  67.5 2.7 %collective-permute-start.34 = (bf16[8,64,128]{2,1,0:T(8,128)(2,1)S(1)}, bf16[8,64,128]{2,1,0:T(8,128)(2,1)S(1)}, u32[]{:S(2)}, u32[]{:S(2)}) collective-permute-start(bf16[8,64,128]{2,1,0:T(8,128)(2,1)S(1)} %get-tuple-element.82.refs_2_.refs_3_), channel_id=1, source_target_pairs={{0,1},{1,0},{2,3},{3,2},{4,5},{5,4},{6,7},{7,6},{8,9},{9,8},{10,11... | collective-permute-start | bytes 393224 | tf_op jit(solution)/shard_map/ppermute | solution.py:39
  67.6 9.6 %collective-permute-start.42 = (bf16[8,64,128]{2,1,0:T(8,128)(2,1)S(1)}, bf16[8,64,128]{2,1,0:T(8,128)(2,1)S(1)}, u32[]{:S(2)}, u32[]{:S(2)}) collective-permute-start(bf16[8,64,128]{2,1,0:T(8,128)(2,1)S(1)} %get-tuple-element.82.refs_2_.refs_3_), channel_id=1, source_target_pairs={{0,16},{8,24},{16,0},{24,8},{1,17},{9,25},{17,1},{25,9},{2,18},{10... | collective-permute-start | bytes 393224 | tf_op jit(solution)/shard_map/ppermute | solution.py:39
  70.1 6.0 %collective-permute-start.41 = (bf16[7,64,128]{2,1,0:T(8,128)(2,1)S(1)}, bf16[7,64,128]{2,1,0:T(8,128)(2,1)S(1)}, u32[]{:S(2)}, u32[]{:S(2)}) collective-permute-start(bf16[7,64,128]{2,1,0:T(8,128)(2,1)S(1)} %slice.22), channel_id=1, source_target_pairs={{0,8},{8,0},{16,24},{24,16},{1,9},{9,1},{17,25},{25,17},{2,10},{10... | collective-permute-start | bytes 344072 | tf_op jit(solution)/shard_map/ppermute | solution.py:39
  70.2 8.3 %collective-permute-start.35 = (bf16[8,64,128]{2,1,0:T(8,128)(2,1)S(1)}, bf16[8,64,128]{2,1,0:T(8,128)(2,1)S(1)}, u32[]{:S(2)}, u32[]{:S(2)}) collective-permute-start(bf16[8,64,128]{2,1,0:T(8,128)(2,1)S(1)} %get-tuple-element.82.refs_2_.refs_3_), channel_id=1, source_target_pairs={{0,6},{1,7},{2,4},{3,5},{4,2},{5,3},{6,0},{7,1},{8,14},{9,15},{10,... | collective-permute-start | bytes 393224 | tf_op jit(solution)/shard_map/ppermute | solution.py:39
  72.8 6.8 %collective-permute-start.36 = (bf16[8,64,128]{2,1,0:T(8,128)(2,1)S(1)}, bf16[8,64,128]{2,1,0:T(8,128)(2,1)S(1)}, u32[]{:S(2)}, u32[]{:S(2)}) collective-permute-start(bf16[8,64,128]{2,1,0:T(8,128)(2,1)S(1)} %get-tuple-element.82.refs_2_.refs_3_), channel_id=1, source_target_pairs={{0,4},{1,5},{2,6},{3,7},{4,0},{5,1},{6,2},{7,3},{8,12},{9,13},{10,... | collective-permute-start | bytes 393224 | tf_op jit(solution)/shard_map/ppermute | solution.py:39
  73.3 6.4 %collective-permute-start.37 = (bf16[8,64,128]{2,1,0:T(8,128)(2,1)S(1)}, bf16[8,64,128]{2,1,0:T(8,128)(2,1)S(1)}, u32[]{:S(2)}, u32[]{:S(2)}) collective-permute-start(bf16[8,64,128]{2,1,0:T(8,128)(2,1)S(1)} %get-tuple-element.82.refs_2_.refs_3_), channel_id=1, source_target_pairs={{0,2},{1,3},{2,0},{3,1},{4,6},{5,7},{6,4},{7,5},{8,10},{9,11},{10,... | collective-permute-start | bytes 393224 | tf_op jit(solution)/shard_map/ppermute | solution.py:39
  77.2 5.4 %collective-permute-start.43 = (bf16[9,64,128]{2,1,0:T(8,128)(2,1)S(1)}, bf16[9,64,128]{2,1,0:T(8,128)(2,1)S(1)}, u32[]{:S(2)}, u32[]{:S(2)}) collective-permute-start(bf16[9,64,128]{2,1,0:T(8,128)(2,1)S(1)} %pad_maximum_fusion.2), channel_id=1, source_target_pairs={{0,8},{8,0},{16,24},{24,16},{1,9},{9,1},{17,25},{25,17},{2,10},{10... | collective-permute-start | bytes 442376 | tf_op jit(solution)/shard_map/ppermute | solution.py:39
  78.6 1.5 %collective-permute-start.38 = (bf16[8,64,128]{2,1,0:T(8,128)(2,1)S(1)}, bf16[8,64,128]{2,1,0:T(8,128)(2,1)S(1)}, u32[]{:S(2)}, u32[]{:S(2)}) collective-permute-start(bf16[8,64,128]{2,1,0:T(8,128)(2,1)S(1)} %collective-permute-done.35.refs_3_), channel_id=1, source_target_pairs={{0,1},{1,0},{2,3},{3,2},{4,5},{5,4},{6,7},{7,6},{8,9},{9,8},{10,11... | collective-permute-start | bytes 393224 | tf_op jit(solution)/shard_map/ppermute | solution.py:39
  79.7 1.4 %collective-permute-start.40 = (bf16[8,64,128]{2,1,0:T(8,128)(2,1)S(1)}, bf16[8,64,128]{2,1,0:T(8,128)(2,1)S(1)}, u32[]{:S(2)}, u32[]{:S(2)}) collective-permute-start(bf16[8,64,128]{2,1,0:T(8,128)(2,1)S(1)} %collective-permute-done.37.refs_5_), channel_id=1, source_target_pairs={{0,1},{1,0},{2,3},{3,2},{4,5},{5,4},{6,7},{7,6},{8,9},{9,8},{10,11... | collective-permute-start | bytes 393224 | tf_op jit(solution)/shard_map/ppermute | solution.py:39
  85.1 4.7 %collective-permute-start.45 = (f32[40,128]{1,0:T(8,128)S(1)}, f32[40,128]{1,0:T(8,128)S(1)}, u32[]{:S(2)}, u32[]{:S(2)}) collective-permute-start(f32[40,128]{1,0:T(8,128)S(1)} %add.12), channel_id=1, source_target_pairs={{0,6},{1,7},{2,4},{3,5},{4,2},{5,3},{6,0},{7,1},{8,14},{9,15},{10,... | collective-permute-start | bytes 61448 | tf_op jit(solution)/shard_map/ppermute | solution.py:39
  87.3 3.8 %collective-permute-start.46 = (f32[40,128]{1,0:T(8,128)S(1)}, f32[40,128]{1,0:T(8,128)S(1)}, u32[]{:S(2)}, u32[]{:S(2)}) collective-permute-start(f32[40,128]{1,0:T(8,128)S(1)} %add.12), channel_id=1, source_target_pairs={{0,4},{1,5},{2,6},{3,7},{4,0},{5,1},{6,2},{7,3},{8,12},{9,13},{10,... | collective-permute-start | bytes 61448 | tf_op jit(solution)/shard_map/ppermute | solution.py:39
  88.1 3.8 %collective-permute-start.47 = (f32[40,128]{1,0:T(8,128)S(1)}, f32[40,128]{1,0:T(8,128)S(1)}, u32[]{:S(2)}, u32[]{:S(2)}) collective-permute-start(f32[40,128]{1,0:T(8,128)S(1)} %add.12), channel_id=1, source_target_pairs={{0,2},{1,3},{2,0},{3,1},{4,6},{5,7},{6,4},{7,5},{8,10},{9,11},{10,... | collective-permute-start | bytes 61448 | tf_op jit(solution)/shard_map/ppermute | solution.py:39
  91.9 5.8 %collective-permute-start.48 = (f32[40,128]{1,0:T(8,128)S(1)}, f32[40,128]{1,0:T(8,128)S(1)}, u32[]{:S(2)}, u32[]{:S(2)}) collective-permute-start(f32[40,128]{1,0:T(8,128)S(1)} %add_add_fusion.refs_1_), channel_id=1, source_target_pairs={{0,24},{8,16},{16,8},{24,0},{1,25},{9,17},{17,9},{25,1},{2,26},{10... | collective-permute-start | bytes 61448 | tf_op jit(solution)/shard_map/ppermute | solution.py:39
  94.3 4.7 %collective-permute-start.49 = (f32[40,128]{1,0:T(8,128)S(1)}, f32[40,128]{1,0:T(8,128)S(1)}, u32[]{:S(2)}, u32[]{:S(2)}) collective-permute-start(f32[40,128]{1,0:T(8,128)S(1)} %add_add_fusion.refs_1_), channel_id=1, source_target_pairs={{0,16},{8,24},{16,0},{24,8},{1,17},{9,25},{17,1},{25,9},{2,18},{10... | collective-permute-start | bytes 61448 | tf_op jit(solution)/shard_map/ppermute | solution.py:39
  94.7 4.3 %collective-permute-start.50 = (f32[40,128]{1,0:T(8,128)S(1)}, f32[40,128]{1,0:T(8,128)S(1)}, u32[]{:S(2)}, u32[]{:S(2)}) collective-permute-start(f32[40,128]{1,0:T(8,128)S(1)} %add_add_fusion.refs_1_), channel_id=1, source_target_pairs={{0,8},{8,0},{16,24},{24,16},{1,9},{9,1},{17,25},{25,17},{2,10},{10... | collective-permute-start | bytes 61448 | tf_op jit(solution)/shard_map/ppermute | solution.py:39
  (8 other events, 21.2 us)

commit v24 on v21

--- a/solution.py
+++ b/solution.py
@@ -497,14 +497,14 @@
         [table, left, gram, *col_parts],
         2 * vectors_n * spread[0] * spread[1],
     )
-    sums = sums + trade(sums, "col", 1)
     sums = tree_sum([*exchange([sums] * (chips_n - 1), "col", 2)[::-1], sums])
+    sums = tree_sum([*exchange([sums] * (rows_n - 1), "row")[::-1], sums])
     return call(
         functools.partial(last_kernel, total_nodes),
         [vector_shape, jax.ShapeDtypeStruct((vectors_n, vectors_n), F32)],
         [],
         24,
-        [filtered, sums, *exchange([sums] * (rows_n - 1), "row")[::-1]],
+        [filtered, sums, trade(sums, "col", 1)],
     )
 
 

time: 99.3 us -> 99.4 us (level)
  no operation moved by 1% of the time
where the time goes in v24:
time: 99.4 us; the launch traced here: 99.2 us
  starting transfers between devices  54.8 us (55%)
  waiting for transfers between devices  26.9 us (27%)
  Pallas kernels  12.9 us (13%)
  local copies, waits for them, and re-layouts  3.59 us (4%)
    ppermute x51, starting transfers between devices, trade(): return lax.ppermute(part, axis, [(i, i ^ d) for i in range(n)])  54.8 us
    ppermute x51, waiting for transfers between devices, trade(): return lax.ppermute(part, axis, [(i, i ^ d) for i in range(n)])  26.9 us
    pallas_call x17, Pallas kernels, call(): pl.pallas_call(lambda *refs: kernel(*refs[len(after):]), out_shape=jax.tr...  12.9 us
    unnamed x10, local copies, waits for them, and re-layouts  3.49 us
  transfers between devices with their start and end apart: 51, of which 25 were waited for; matrix products, arithmetic and copies ran while one was open for 0% of the time, Pallas kernels for 5%

profile of v24, /device:TPU:0, one launch (start us, length us, event | category | flops | bytes accessed | tf_op | source)
XLA Modules:
  0.0 99.2 jit_solution(10072216836896604183)
XLA Ops:
  0.6 0.9 copy-done
  1.6 4.1 %collective-permute-start.8 = (bf16[8,64,128]{2,1,0:T(8,128)(2,1)S(1)}, bf16[8,64,128]{2,1,0:T(8,128)(2,1)S(1)}, u32[]{:S(2)}, u32[]{:S(2)}) collective-permute-start(bf16[8,64,128]{2,1,0:T(8,128)(2,1)S(1)} %shard_map.61.refs_2_.refs_3_), channel_id=1, source_target_pairs={{0,16},{8,24},{16,0},{24,8},{1,17},{9,25},{17,1},{25,9},{2,18},{10... | collective-permute-start | bytes 393224 | tf_op jit(solution)/shard_map/ppermute | solution.py:39
  5.7 1.6 %collective-permute-start.7 = (bf16[7,64,128]{2,1,0:T(8,128)(2,1)S(1)}, bf16[7,64,128]{2,1,0:T(8,128)(2,1)S(1)}, u32[]{:S(2)}, u32[]{:S(2)}) collective-permute-start(bf16[7,64,128]{2,1,0:T(8,128)(2,1)S(1)} %slice.24), channel_id=1, source_target_pairs={{0,8},{8,0},{16,24},{24,16},{1,9},{9,1},{17,25},{25,17},{2,10},{10... | collective-permute-start | bytes 344072 | tf_op jit(solution)/shard_map/ppermute | solution.py:39
  7.4 2.4 %collective-permute-start = (bf16[8,64,128]{2,1,0:T(8,128)(2,1)S(1)}, bf16[8,64,128]{2,1,0:T(8,128)(2,1)S(1)}, u32[]{:S(2)}, u32[]{:S(2)}) collective-permute-start(bf16[8,64,128]{2,1,0:T(8,128)(2,1)S(1)} %shard_map.61.refs_2_.refs_3_), channel_id=1, source_target_pairs={{0,6},{1,7},{2,4},{3,5},{4,2},{5,3},{6,0},{7,1},{8,14},{9,15},{10,... | collective-permute-start | bytes 393224 | tf_op jit(solution)/shard_map/ppermute | solution.py:39
  12.6 0.9 collective-permute-start.9
  14.0 1.7 %collective-permute-done.1.refs_4_ = bf16[8,64,128]{2,1,0:T(8,128)(2,1)S(1)} collective-permute-done((bf16[8,64,128]{2,1,0:T(8,128)(2,1)S(1)}, bf16[8,64,128]{2,1,0:T(8,128)(2,1)S(1)}, u32[]{:S(2)}, u32[]{:S(2)}) %collective-permute-start.1) | collective-permute-done | bytes 131104 | tf_op jit(solution)/shard_map/ppermute | solution.py:39
  16.3 1.2 %copy-done.2 = bf16[1,1,32,128,128]{4,3,2,1,0:T(8,128)(2,1)S(1)} copy-done((bf16[1,1,32,128,128]{4,3,2,1,0:T(8,128)(2,1)S(1)}, bf16[1,1,32,128,128]{4,3,2,1,0:T(8,128)(2,1)}, u32[]{:S(2)}) %copy-start.2) | copy-done | bytes 1048600
  17.6 1.1 %shard_map.63 = (f32[8,80,128]{2,1,0:T(8,128)S(1)}, f32[32,80,128]{2,1,0:T(8,128)S(1)}, bf16[528,128]{1,0:T(8,128)(2,1)S(1)}, bf16[528,128]{1,0:T(8,128)(2,1)S(1)}, bf16[528,128]{1,0:T(8,128)(2,1)S(1)}) custom-call(s32[3,32]{1,0:T(4,128)S(1)} %shard_map.59.refs_0_.refs_1_, ...), custom_call_target="tpu_custom_call", output_to_operand_aliasing={{1}: (10, {})} | custom-call | flops 67108864 | bytes 3408256 | tf_op jit(solution)/shard_map/pallas_call | solution.py:25
  18.8 1.5 %shard_map.64 = (f32[64,80,128]{2,1,0:T(8,128)S(1)}, bf16[4,528,128]{2,1,0:T(8,128)(2,1)S(1)}) custom-call(f32[8,80,128]{2,1,0:T(8,128)S(1)} %get-tuple-element.39.refs_0_.refs_3_, s32[3,32]{1,0:T(4,128)S(1)} %shard_map.59.refs_0_.refs_1_, bf16[32,128,128]{2,1,0:T(8,128)(2,1)S(1)} %shard_map.60.refs_1_.refs_2_, ...), custom_call_target="tpu_custom_call", output_to_operand_aliasing={{0}: (7, {})} | custom-call | flops 67108864 | bytes 4194688 | tf_op jit(solution)/shard_map/pallas_call | solution.py:25
  20.9 2.7 %collective-permute-start.15 = (bf16[528,128]{1,0:T(8,128)(2,1)S(1)}, bf16[528,128]{1,0:T(8,128)(2,1)S(1)}, u32[]{:S(2)}, u32[]{:S(2)}) collective-permute-start(bf16[528,128]{1,0:T(8,128)(2,1)S(1)} %get-tuple-element.51), channel_id=1, source_target_pairs={{0,16},{8,24},{16,0},{24,8},{1,17},{9,25},{17,1},{25,9},{2,18},{10... | collective-permute-start | bytes 405512 | tf_op jit(solution)/shard_map/ppermute | solution.py:39
  23.6 1.2 %collective-permute-start.16 = (bf16[528,128]{1,0:T(8,128)(2,1)S(1)}, bf16[528,128]{1,0:T(8,128)(2,1)S(1)}, u32[]{:S(2)}, u32[]{:S(2)}) collective-permute-start(bf16[528,128]{1,0:T(8,128)(2,1)S(1)} %get-tuple-element.52), channel_id=1, source_target_pairs={{0,24},{8,16},{16,8},{24,0},{1,25},{9,17},{17,9},{25,1},{2,26},{10... | collective-permute-start | bytes 405512 | tf_op jit(solution)/shard_map/ppermute | solution.py:39
  24.9 1.8 %collective-permute-start.11 = (bf16[528,128]{1,0:T(8,128)(2,1)S(1)}, bf16[528,128]{1,0:T(8,128)(2,1)S(1)}, u32[]{:S(2)}, u32[]{:S(2)}) collective-permute-start(bf16[528,128]{1,0:T(8,128)(2,1)S(1)} %get-tuple-element.47), channel_id=1, source_target_pairs={{0,6},{1,7},{2,4},{3,5},{4,2},{5,3},{6,0},{7,1},{8,14},{9,15},{10,... | collective-permute-start | bytes 405512 | tf_op jit(solution)/shard_map/ppermute | solution.py:39
  26.8 1.2 %collective-permute-start.12 = (bf16[528,128]{1,0:T(8,128)(2,1)S(1)}, bf16[528,128]{1,0:T(8,128)(2,1)S(1)}, u32[]{:S(2)}, u32[]{:S(2)}) collective-permute-start(bf16[528,128]{1,0:T(8,128)(2,1)S(1)} %get-tuple-element.48), channel_id=1, source_target_pairs={{0,4},{1,5},{2,6},{3,7},{4,0},{5,1},{6,2},{7,3},{8,12},{9,13},{10,... | collective-permute-start | bytes 405512 | tf_op jit(solution)/shard_map/ppermute | solution.py:39
  28.0 0.8 collective-permute-done.14.refs_7_
  28.8 1.5 %collective-permute-start.13 = (bf16[528,128]{1,0:T(8,128)(2,1)S(1)}, bf16[528,128]{1,0:T(8,128)(2,1)S(1)}, u32[]{:S(2)}, u32[]{:S(2)}) collective-permute-start(bf16[528,128]{1,0:T(8,128)(2,1)S(1)} %get-tuple-element.49), channel_id=1, source_target_pairs={{0,2},{1,3},{2,0},{3,1},{4,6},{5,7},{6,4},{7,5},{8,10},{9,11},{10,... | collective-permute-start | bytes 405512 | tf_op jit(solution)/shard_map/ppermute | solution.py:39
  30.3 3.7 %collective-permute-done.15.refs_8_ = bf16[528,128]{1,0:T(8,128)(2,1)S(1)} collective-permute-done((bf16[528,128]{1,0:T(8,128)(2,1)S(1)}, bf16[528,128]{1,0:T(8,128)(2,1)S(1)}, u32[]{:S(2)}, u32[]{:S(2)}) %collective-permute-start.15) | collective-permute-done | bytes 135200 | tf_op jit(solution)/shard_map/ppermute | solution.py:39
  34.2 3.8 %collective-permute-start.25 = (bf16[8,64,128]{2,1,0:T(8,128)(2,1)S(1)}, bf16[8,64,128]{2,1,0:T(8,128)(2,1)S(1)}, u32[]{:S(2)}, u32[]{:S(2)}) collective-permute-start(bf16[8,64,128]{2,1,0:T(8,128)(2,1)S(1)} %get-tuple-element.55.refs_2_.refs_3_), channel_id=1, source_target_pairs={{0,16},{8,24},{16,0},{24,8},{1,17},{9,25},{17,1},{25,9},{2,18},{10... | collective-permute-start | bytes 393224 | tf_op jit(solution)/shard_map/ppermute | solution.py:39
  38.1 2.5 %collective-permute-start.17 = (bf16[8,64,128]{2,1,0:T(8,128)(2,1)S(1)}, bf16[8,64,128]{2,1,0:T(8,128)(2,1)S(1)}, u32[]{:S(2)}, u32[]{:S(2)}) collective-permute-start(bf16[8,64,128]{2,1,0:T(8,128)(2,1)S(1)} %get-tuple-element.55.refs_2_.refs_3_), channel_id=1, source_target_pairs={{0,6},{1,7},{2,4},{3,5},{4,2},{5,3},{6,0},{7,1},{8,14},{9,15},{10,... | collective-permute-start | bytes 393224 | tf_op jit(solution)/shard_map/ppermute | solution.py:39
  41.9 2.1 %collective-permute-done.24.refs_5_ = bf16[7,64,128]{2,1,0:T(8,128)(2,1)S(1)} collective-permute-done((bf16[7,64,128]{2,1,0:T(8,128)(2,1)S(1)}, bf16[7,64,128]{2,1,0:T(8,128)(2,1)S(1)}, u32[]{:S(2)}, u32[]{:S(2)}) %collective-permute-start.24) | collective-permute-done | bytes 114720 | tf_op jit(solution)/shard_map/ppermute | solution.py:39
  44.0 1.4 %collective-permute-start.26 = (bf16[9,64,128]{2,1,0:T(8,128)(2,1)S(1)}, bf16[9,64,128]{2,1,0:T(8,128)(2,1)S(1)}, u32[]{:S(2)}, u32[]{:S(2)}) collective-permute-start(bf16[9,64,128]{2,1,0:T(8,128)(2,1)S(1)} %pad_maximum_fusion.1), channel_id=1, source_target_pairs={{0,8},{8,0},{16,24},{24,16},{1,9},{9,1},{17,25},{25,17},{2,10},{10... | collective-permute-start | bytes 442376 | tf_op jit(solution)/shard_map/ppermute | solution.py:39
  46.9 0.8 collective-permute-done.22.refs_8_
  47.9 1.0 %shard_map.68 = (f32[8,64,128]{2,1,0:T(8,128)S(1)}, f32[32,64,128]{2,1,0:T(8,128)S(1)}, bf16[512,128]{1,0:T(8,128)(2,1)S(1)}, bf16[512,128]{1,0:T(8,128)(2,1)S(1)}, bf16[512,128]{1,0:T(8,128)(2,1)S(1)}) custom-call(s32[3,32]{1,0:T(4,128)S(1)} %shard_map.59.refs_0_.refs_1_, ...), custom_call_target="tpu_custom_call", output_to_operand_aliasing={{1}: (10, {})} | custom-call | flops 67108864 | bytes 3146112 | tf_op jit(solution)/shard_map/pallas_call | solution.py:25
  49.2 1.4 %shard_map.69 = (f32[64,64,128]{2,1,0:T(8,128)S(1)}, bf16[4,512,128]{2,1,0:T(8,128)(2,1)S(1)}) custom-call(f32[8,64,128]{2,1,0:T(8,128)S(1)} %get-tuple-element.57.refs_0_.refs_4_, s32[3,32]{1,0:T(4,128)S(1)} %shard_map.59.refs_0_.refs_1_, bf16[32,128,128]{2,1,0:T(8,128)(2,1)S(1)} %shard_map.60.refs_1_.refs_2_, ...), custom_call_target="tpu_custom_call", output_to_operand_aliasing={{0}: (7, {})} | custom-call | flops 67108864 | bytes 3670400 | tf_op jit(solution)/shard_map/pallas_call | solution.py:25
  50.8 1.7 %collective-permute-start.31 = (bf16[512,128]{1,0:T(8,128)(2,1)S(1)}, bf16[512,128]{1,0:T(8,128)(2,1)S(1)}, u32[]{:S(2)}, u32[]{:S(2)}) collective-permute-start(bf16[512,128]{1,0:T(8,128)(2,1)S(1)} %get-tuple-element.67), channel_id=1, source_target_pairs={{0,8},{8,0},{16,24},{24,16},{1,9},{9,1},{17,25},{25,17},{2,10},{10... | collective-permute-start | bytes 393224 | tf_op jit(solution)/shard_map/ppermute | solution.py:39
  52.5 0.8 collective-permute-start.32
  53.3 1.9 %collective-permute-start.33 = (bf16[512,128]{1,0:T(8,128)(2,1)S(1)}, bf16[512,128]{1,0:T(8,128)(2,1)S(1)}, u32[]{:S(2)}, u32[]{:S(2)}) collective-permute-start(bf16[512,128]{1,0:T(8,128)(2,1)S(1)} %get-tuple-element.69), channel_id=1, source_target_pairs={{0,24},{8,16},{16,8},{24,0},{1,25},{9,17},{17,9},{25,1},{2,26},{10... | collective-permute-start | bytes 393224 | tf_op jit(solution)/shard_map/ppermute | solution.py:39
  55.3 2.5 %collective-permute-start.28 = (bf16[512,128]{1,0:T(8,128)(2,1)S(1)}, bf16[512,128]{1,0:T(8,128)(2,1)S(1)}, u32[]{:S(2)}, u32[]{:S(2)}) collective-permute-start(bf16[512,128]{1,0:T(8,128)(2,1)S(1)} %get-tuple-element.64), channel_id=1, source_target_pairs={{0,6},{1,7},{2,4},{3,5},{4,2},{5,3},{6,0},{7,1},{8,14},{9,15},{10,... | collective-permute-start | bytes 393224 | tf_op jit(solution)/shard_map/ppermute | solution.py:39
  58.3 1.6 %collective-permute-start.30 = (bf16[512,128]{1,0:T(8,128)(2,1)S(1)}, bf16[512,128]{1,0:T(8,128)(2,1)S(1)}, u32[]{:S(2)}, u32[]{:S(2)}) collective-permute-start(bf16[512,128]{1,0:T(8,128)(2,1)S(1)} %get-tuple-element.66), channel_id=1, source_target_pairs={{0,2},{1,3},{2,0},{3,1},{4,6},{5,7},{6,4},{7,5},{8,10},{9,11},{10,... | collective-permute-start | bytes 393224 | tf_op jit(solution)/shard_map/ppermute | solution.py:39
  59.9 5.4 %collective-permute-done.32.refs_9_ = bf16[512,128]{1,0:T(8,128)(2,1)S(1)} collective-permute-done((bf16[512,128]{1,0:T(8,128)(2,1)S(1)}, bf16[512,128]{1,0:T(8,128)(2,1)S(1)}, u32[]{:S(2)}, u32[]{:S(2)}) %collective-permute-start.32) | collective-permute-done | bytes 131104 | tf_op jit(solution)/shard_map/ppermute | solution.py:39
  65.6 2.6 %collective-permute-start.42 = (bf16[8,64,128]{2,1,0:T(8,128)(2,1)S(1)}, bf16[8,64,128]{2,1,0:T(8,128)(2,1)S(1)}, u32[]{:S(2)}, u32[]{:S(2)}) collective-permute-start(bf16[8,64,128]{2,1,0:T(8,128)(2,1)S(1)} %get-tuple-element.71.refs_2_.refs_3_), channel_id=1, source_target_pairs={{0,16},{8,24},{16,0},{24,8},{1,17},{9,25},{17,1},{25,9},{2,18},{10... | collective-permute-start | bytes 393224 | tf_op jit(solution)/shard_map/ppermute | solution.py:39
  68.3 2.5 %collective-permute-start.34 = (bf16[8,64,128]{2,1,0:T(8,128)(2,1)S(1)}, bf16[8,64,128]{2,1,0:T(8,128)(2,1)S(1)}, u32[]{:S(2)}, u32[]{:S(2)}) collective-permute-start(bf16[8,64,128]{2,1,0:T(8,128)(2,1)S(1)} %get-tuple-element.71.refs_2_.refs_3_), channel_id=1, source_target_pairs={{0,6},{1,7},{2,4},{3,5},{4,2},{5,3},{6,0},{7,1},{8,14},{9,15},{10,... | collective-permute-start | bytes 393224 | tf_op jit(solution)/shard_map/ppermute | solution.py:39
  72.5 1.4 %collective-permute-done.41.refs_5_ = bf16[7,64,128]{2,1,0:T(8,128)(2,1)S(1)} collective-permute-done((bf16[7,64,128]{2,1,0:T(8,128)(2,1)S(1)}, bf16[7,64,128]{2,1,0:T(8,128)(2,1)S(1)}, u32[]{:S(2)}, u32[]{:S(2)}) %collective-permute-start.41) | collective-permute-done | bytes 114720 | tf_op jit(solution)/shard_map/ppermute | solution.py:39
  74.3 1.0 collective-permute-start.43
  76.9 0.8 collective-permute-done.39.refs_8_
  77.9 1.0 shard_map.72.refs_1_
  79.5 1.2 %shard_map.74 = f32[40,128]{1,0:T(8,128)S(1)} custom-call(s32[3,32]{1,0:T(4,128)S(1)} %shard_map.59.refs_0_.refs_1_, bf16[64,4096]{1,0:T(8,128)(2,1)S(1)} %shard_map.72.refs_1_, f32[64,128]{1,0:T(8,128)S(1)} %shard_map.73.refs_2_, bf16[8,64,128]{2,1,0:T(8,128)(2,1)S(1)} %get-tuple-element.71.refs_2_.refs_3_, ...), custom_call_target="tpu_custom_call" | custom-call | flops 33554432 | bytes 1081728 | tf_op jit(solution)/shard_map/pallas_call | solution.py:25
  80.7 2.1 %collective-permute-start.44 = (f32[40,128]{1,0:T(8,128)S(1)}, f32[40,128]{1,0:T(8,128)S(1)}, u32[]{:S(2)}, u32[]{:S(2)}) collective-permute-start(f32[40,128]{1,0:T(8,128)S(1)} %shard_map.74), channel_id=1, source_target_pairs={{0,6},{1,7},{2,4},{3,5},{4,2},{5,3},{6,0},{7,1},{8,14},{9,15},{10,... | collective-permute-start | bytes 61448 | tf_op jit(solution)/shard_map/ppermute | solution.py:39
  82.8 0.9 collective-permute-start.45
  84.2 1.2 %collective-permute-done.44 = f32[40,128]{1,0:T(8,128)S(1)} collective-permute-done((f32[40,128]{1,0:T(8,128)S(1)}, f32[40,128]{1,0:T(8,128)S(1)}, u32[]{:S(2)}, u32[]{:S(2)}) %collective-permute-start.44) | collective-permute-done | bytes 20512 | tf_op jit(solution)/shard_map/ppermute | solution.py:39
  85.4 1.1 %collective-permute-done.45 = f32[40,128]{1,0:T(8,128)S(1)} collective-permute-done((f32[40,128]{1,0:T(8,128)S(1)}, f32[40,128]{1,0:T(8,128)S(1)}, u32[]{:S(2)}, u32[]{:S(2)}) %collective-permute-start.45) | collective-permute-done | bytes 20512 | tf_op jit(solution)/shard_map/ppermute | solution.py:39
  86.5 0.9 collective-permute-done.46
  87.4 1.9 %collective-permute-start.47 = (f32[40,128]{1,0:T(8,128)S(1)}, f32[40,128]{1,0:T(8,128)S(1)}, u32[]{:S(2)}, u32[]{:S(2)}) collective-permute-start(f32[40,128]{1,0:T(8,128)S(1)} %add_add_fusion.1), channel_id=1, source_target_pairs={{0,24},{8,16},{16,8},{24,0},{1,25},{9,17},{17,9},{25,1},{2,26},{10... | collective-permute-start | bytes 61448 | tf_op jit(solution)/shard_map/ppermute | solution.py:39
  89.3 0.9 collective-permute-start.48
  90.2 1.7 %collective-permute-start.49 = (f32[40,128]{1,0:T(8,128)S(1)}, f32[40,128]{1,0:T(8,128)S(1)}, u32[]{:S(2)}, u32[]{:S(2)}) collective-permute-start(f32[40,128]{1,0:T(8,128)S(1)} %add_add_fusion.1), channel_id=1, source_target_pairs={{0,8},{8,0},{16,24},{24,16},{1,9},{9,1},{17,25},{25,17},{2,10},{10... | collective-permute-start | bytes 61448 | tf_op jit(solution)/shard_map/ppermute | solution.py:39
  91.9 1.2 %collective-permute-done.47 = f32[40,128]{1,0:T(8,128)S(1)} collective-permute-done((f32[40,128]{1,0:T(8,128)S(1)}, f32[40,128]{1,0:T(8,128)S(1)}, u32[]{:S(2)}, u32[]{:S(2)}) %collective-permute-start.47) | collective-permute-done | bytes 20512 | tf_op jit(solution)/shard_map/ppermute | solution.py:39
  93.1 1.1 %collective-permute-done.48 = f32[40,128]{1,0:T(8,128)S(1)} collective-permute-done((f32[40,128]{1,0:T(8,128)S(1)}, f32[40,128]{1,0:T(8,128)S(1)}, u32[]{:S(2)}, u32[]{:S(2)}) %collective-permute-start.48) | collective-permute-done | bytes 20512 | tf_op jit(solution)/shard_map/ppermute | solution.py:39
  94.3 1.2 %collective-permute-done.50.refs_2_ = f32[40,128]{1,0:T(8,128)S(1)} collective-permute-done((f32[40,128]{1,0:T(8,128)S(1)}, f32[40,128]{1,0:T(8,128)S(1)}, u32[]{:S(2)}, u32[]{:S(2)}) %collective-permute-start.50) | collective-permute-done | bytes 20512 | tf_op jit(solution)/shard_map/ppermute | solution.py:39
  95.5 3.8 %shard_map.75 = (f32[64,1024]{1,0:T(8,128)}, f32[64,64]{1,0:T(8,128)}) custom-call(f32[64,1024]{1,0:T(8,128)S(1)} %get-tuple-element.70.refs_0_, f32[40,128]{1,0:T(8,128)S(1)} %add_add_fusion.refs_1_, f32[40,128]{1,0:T(8,128)S(1)} %collective-permute-done.50.refs_2_), custom_call_target="tpu_custom_call" | custom-call | bytes 303104 | tf_op jit(solution)/shard_map/pallas_call | solution.py:25
  (94 shorter events, 14.4 us)
Async XLA Ops:
  1.6 11.0 %collective-permute-start.8 = (bf16[8,64,128]{2,1,0:T(8,128)(2,1)S(1)}, bf16[8,64,128]{2,1,0:T(8,128)(2,1)S(1)}, u32[]{:S(2)}, u32[]{:S(2)}) collective-permute-start(bf16[8,64,128]{2,1,0:T(8,128)(2,1)S(1)} %shard_map.61.refs_2_.refs_3_), channel_id=1, source_target_pairs={{0,16},{8,24},{16,0},{24,8},{1,17},{9,25},{17,1},{25,9},{2,18},{10... | collective-permute-start | bytes 393224 | tf_op jit(solution)/shard_map/ppermute | solution.py:39
  5.7 6.9 %collective-permute-start.7 = (bf16[7,64,128]{2,1,0:T(8,128)(2,1)S(1)}, bf16[7,64,128]{2,1,0:T(8,128)(2,1)S(1)}, u32[]{:S(2)}, u32[]{:S(2)}) collective-permute-start(bf16[7,64,128]{2,1,0:T(8,128)(2,1)S(1)} %slice.24), channel_id=1, source_target_pairs={{0,8},{8,0},{16,24},{24,16},{1,9},{9,1},{17,25},{25,17},{2,10},{10... | collective-permute-start | bytes 344072 | tf_op jit(solution)/shard_map/ppermute | solution.py:39
  7.4 6.6 %collective-permute-start = (bf16[8,64,128]{2,1,0:T(8,128)(2,1)S(1)}, bf16[8,64,128]{2,1,0:T(8,128)(2,1)S(1)}, u32[]{:S(2)}, u32[]{:S(2)}) collective-permute-start(bf16[8,64,128]{2,1,0:T(8,128)(2,1)S(1)} %shard_map.61.refs_2_.refs_3_), channel_id=1, source_target_pairs={{0,6},{1,7},{2,4},{3,5},{4,2},{5,3},{6,0},{7,1},{8,14},{9,15},{10,... | collective-permute-start | bytes 393224 | tf_op jit(solution)/shard_map/ppermute | solution.py:39
  9.8 5.9 %collective-permute-start.1 = (bf16[8,64,128]{2,1,0:T(8,128)(2,1)S(1)}, bf16[8,64,128]{2,1,0:T(8,128)(2,1)S(1)}, u32[]{:S(2)}, u32[]{:S(2)}) collective-permute-start(bf16[8,64,128]{2,1,0:T(8,128)(2,1)S(1)} %shard_map.61.refs_2_.refs_3_), channel_id=1, source_target_pairs={{0,4},{1,5},{2,6},{3,7},{4,0},{5,1},{6,2},{7,3},{8,12},{9,13},{10,... | collective-permute-start | bytes 393224 | tf_op jit(solution)/shard_map/ppermute | solution.py:39
  10.3 5.5 %collective-permute-start.2 = (bf16[8,64,128]{2,1,0:T(8,128)(2,1)S(1)}, bf16[8,64,128]{2,1,0:T(8,128)(2,1)S(1)}, u32[]{:S(2)}, u32[]{:S(2)}) collective-permute-start(bf16[8,64,128]{2,1,0:T(8,128)(2,1)S(1)} %shard_map.61.refs_2_.refs_3_), channel_id=1, source_target_pairs={{0,2},{1,3},{2,0},{3,1},{4,6},{5,7},{6,4},{7,5},{8,10},{9,11},{10,... | collective-permute-start | bytes 393224 | tf_op jit(solution)/shard_map/ppermute | solution.py:39
  12.6 6.1 %collective-permute-start.9 = (bf16[9,64,128]{2,1,0:T(8,128)(2,1)S(1)}, bf16[9,64,128]{2,1,0:T(8,128)(2,1)S(1)}, u32[]{:S(2)}, u32[]{:S(2)}) collective-permute-start(bf16[9,64,128]{2,1,0:T(8,128)(2,1)S(1)} %pad_maximum_fusion), channel_id=1, source_target_pairs={{0,8},{8,0},{16,24},{24,16},{1,9},{9,1},{17,25},{25,17},{2,10},{10... | collective-permute-start | bytes 442376 | tf_op jit(solution)/shard_map/ppermute | solution.py:39
  13.5 4.1 %collective-permute-start.3 = (bf16[8,64,128]{2,1,0:T(8,128)(2,1)S(1)}, bf16[8,64,128]{2,1,0:T(8,128)(2,1)S(1)}, u32[]{:S(2)}, u32[]{:S(2)}) collective-permute-start(bf16[8,64,128]{2,1,0:T(8,128)(2,1)S(1)} %shard_map.61.refs_2_.refs_3_), channel_id=1, source_target_pairs={{0,1},{1,0},{2,3},{3,2},{4,5},{5,4},{6,7},{7,6},{8,9},{9,8},{10,11... | collective-permute-start | bytes 393224 | tf_op jit(solution)/shard_map/ppermute | solution.py:39
  13.9 3.7 %collective-permute-start.4 = (bf16[8,64,128]{2,1,0:T(8,128)(2,1)S(1)}, bf16[8,64,128]{2,1,0:T(8,128)(2,1)S(1)}, u32[]{:S(2)}, u32[]{:S(2)}) collective-permute-start(bf16[8,64,128]{2,1,0:T(8,128)(2,1)S(1)} %collective-permute-done.refs_3_), channel_id=1, source_target_pairs={{0,1},{1,0},{2,3},{3,2},{4,5},{5,4},{6,7},{7,6},{8,9},{9,8},{10,11... | collective-permute-start | bytes 393224 | tf_op jit(solution)/shard_map/ppermute | solution.py:39
  15.7 1.8 %collective-permute-start.5 = (bf16[8,64,128]{2,1,0:T(8,128)(2,1)S(1)}, bf16[8,64,128]{2,1,0:T(8,128)(2,1)S(1)}, u32[]{:S(2)}, u32[]{:S(2)}) collective-permute-start(bf16[8,64,128]{2,1,0:T(8,128)(2,1)S(1)} %collective-permute-done.1.refs_4_), channel_id=1, source_target_pairs={{0,1},{1,0},{2,3},{3,2},{4,5},{5,4},{6,7},{7,6},{8,9},{9,8},{10,11... | collective-permute-start | bytes 393224 | tf_op jit(solution)/shard_map/ppermute | solution.py:39
  15.8 1.8 %collective-permute-start.6 = (bf16[8,64,128]{2,1,0:T(8,128)(2,1)S(1)}, bf16[8,64,128]{2,1,0:T(8,128)(2,1)S(1)}, u32[]{:S(2)}, u32[]{:S(2)}) collective-permute-start(bf16[8,64,128]{2,1,0:T(8,128)(2,1)S(1)} %collective-permute-done.2.refs_5_), channel_id=1, source_target_pairs={{0,1},{1,0},{2,3},{3,2},{4,5},{5,4},{6,7},{7,6},{8,9},{9,8},{10,11... | collective-permute-start | bytes 393224 | tf_op jit(solution)/shard_map/ppermute | solution.py:39
  20.3 4.5 %collective-permute-start.10 = (bf16[4,528,128]{2,1,0:T(8,128)(2,1)S(1)}, bf16[4,528,128]{2,1,0:T(8,128)(2,1)S(1)}, u32[]{:S(2)}, u32[]{:S(2)}) collective-permute-start(bf16[4,528,128]{2,1,0:T(8,128)(2,1)S(1)} %get-tuple-element.44), channel_id=1, source_target_pairs={{0,1},{1,0},{2,3},{3,2},{4,5},{5,4},{6,7},{7,6},{8,9},{9,8},{10,11... | collective-permute-start | bytes 1622024 | tf_op jit(solution)/shard_map/ppermute | solution.py:39
  20.4 8.4 %collective-permute-start.14 = (bf16[528,128]{1,0:T(8,128)(2,1)S(1)}, bf16[528,128]{1,0:T(8,128)(2,1)S(1)}, u32[]{:S(2)}, u32[]{:S(2)}) collective-permute-start(bf16[528,128]{1,0:T(8,128)(2,1)S(1)} %get-tuple-element.50), channel_id=1, source_target_pairs={{0,8},{8,0},{16,24},{24,16},{1,9},{9,1},{17,25},{25,17},{2,10},{10... | collective-permute-start | bytes 405512 | tf_op jit(solution)/shard_map/ppermute | solution.py:39
  20.9 13.1 %collective-permute-start.15 = (bf16[528,128]{1,0:T(8,128)(2,1)S(1)}, bf16[528,128]{1,0:T(8,128)(2,1)S(1)}, u32[]{:S(2)}, u32[]{:S(2)}) collective-permute-start(bf16[528,128]{1,0:T(8,128)(2,1)S(1)} %get-tuple-element.51), channel_id=1, source_target_pairs={{0,16},{8,24},{16,0},{24,8},{1,17},{9,25},{17,1},{25,9},{2,18},{10... | collective-permute-start | bytes 405512 | tf_op jit(solution)/shard_map/ppermute | solution.py:39
  23.6 10.4 %collective-permute-start.16 = (bf16[528,128]{1,0:T(8,128)(2,1)S(1)}, bf16[528,128]{1,0:T(8,128)(2,1)S(1)}, u32[]{:S(2)}, u32[]{:S(2)}) collective-permute-start(bf16[528,128]{1,0:T(8,128)(2,1)S(1)} %get-tuple-element.52), channel_id=1, source_target_pairs={{0,24},{8,16},{16,8},{24,0},{1,25},{9,17},{17,9},{25,1},{2,26},{10... | collective-permute-start | bytes 405512 | tf_op jit(solution)/shard_map/ppermute | solution.py:39
  24.9 9.1 %collective-permute-start.11 = (bf16[528,128]{1,0:T(8,128)(2,1)S(1)}, bf16[528,128]{1,0:T(8,128)(2,1)S(1)}, u32[]{:S(2)}, u32[]{:S(2)}) collective-permute-start(bf16[528,128]{1,0:T(8,128)(2,1)S(1)} %get-tuple-element.47), channel_id=1, source_target_pairs={{0,6},{1,7},{2,4},{3,5},{4,2},{5,3},{6,0},{7,1},{8,14},{9,15},{10,... | collective-permute-start | bytes 405512 | tf_op jit(solution)/shard_map/ppermute | solution.py:39
  26.8 7.3 %collective-permute-start.12 = (bf16[528,128]{1,0:T(8,128)(2,1)S(1)}, bf16[528,128]{1,0:T(8,128)(2,1)S(1)}, u32[]{:S(2)}, u32[]{:S(2)}) collective-permute-start(bf16[528,128]{1,0:T(8,128)(2,1)S(1)} %get-tuple-element.48), channel_id=1, source_target_pairs={{0,4},{1,5},{2,6},{3,7},{4,0},{5,1},{6,2},{7,3},{8,12},{9,13},{10,... | collective-permute-start | bytes 405512 | tf_op jit(solution)/shard_map/ppermute | solution.py:39
  28.8 5.2 %collective-permute-start.13 = (bf16[528,128]{1,0:T(8,128)(2,1)S(1)}, bf16[528,128]{1,0:T(8,128)(2,1)S(1)}, u32[]{:S(2)}, u32[]{:S(2)}) collective-permute-start(bf16[528,128]{1,0:T(8,128)(2,1)S(1)} %get-tuple-element.49), channel_id=1, source_target_pairs={{0,2},{1,3},{2,0},{3,1},{4,6},{5,7},{6,4},{7,5},{8,10},{9,11},{10,... | collective-permute-start | bytes 405512 | tf_op jit(solution)/shard_map/ppermute | solution.py:39
  34.2 9.7 %collective-permute-start.25 = (bf16[8,64,128]{2,1,0:T(8,128)(2,1)S(1)}, bf16[8,64,128]{2,1,0:T(8,128)(2,1)S(1)}, u32[]{:S(2)}, u32[]{:S(2)}) collective-permute-start(bf16[8,64,128]{2,1,0:T(8,128)(2,1)S(1)} %get-tuple-element.55.refs_2_.refs_3_), channel_id=1, source_target_pairs={{0,16},{8,24},{16,0},{24,8},{1,17},{9,25},{17,1},{25,9},{2,18},{10... | collective-permute-start | bytes 393224 | tf_op jit(solution)/shard_map/ppermute | solution.py:39
  38.0 5.9 %collective-permute-start.24 = (bf16[7,64,128]{2,1,0:T(8,128)(2,1)S(1)}, bf16[7,64,128]{2,1,0:T(8,128)(2,1)S(1)}, u32[]{:S(2)}, u32[]{:S(2)}) collective-permute-start(bf16[7,64,128]{2,1,0:T(8,128)(2,1)S(1)} %slice.20), channel_id=1, source_target_pairs={{0,8},{8,0},{16,24},{24,16},{1,9},{9,1},{17,25},{25,17},{2,10},{10... | collective-permute-start | bytes 344072 | tf_op jit(solution)/shard_map/ppermute | solution.py:39
  38.1 7.2 %collective-permute-start.17 = (bf16[8,64,128]{2,1,0:T(8,128)(2,1)S(1)}, bf16[8,64,128]{2,1,0:T(8,128)(2,1)S(1)}, u32[]{:S(2)}, u32[]{:S(2)}) collective-permute-start(bf16[8,64,128]{2,1,0:T(8,128)(2,1)S(1)} %get-tuple-element.55.refs_2_.refs_3_), channel_id=1, source_target_pairs={{0,6},{1,7},{2,4},{3,5},{4,2},{5,3},{6,0},{7,1},{8,14},{9,15},{10,... | collective-permute-start | bytes 393224 | tf_op jit(solution)/shard_map/ppermute | solution.py:39
  40.6 5.7 %collective-permute-start.18 = (bf16[8,64,128]{2,1,0:T(8,128)(2,1)S(1)}, bf16[8,64,128]{2,1,0:T(8,128)(2,1)S(1)}, u32[]{:S(2)}, u32[]{:S(2)}) collective-permute-start(bf16[8,64,128]{2,1,0:T(8,128)(2,1)S(1)} %get-tuple-element.55.refs_2_.refs_3_), channel_id=1, source_target_pairs={{0,4},{1,5},{2,6},{3,7},{4,0},{5,1},{6,2},{7,3},{8,12},{9,13},{10,... | collective-permute-start | bytes 393224 | tf_op jit(solution)/shard_map/ppermute | solution.py:39
  41.1 5.3 %collective-permute-start.19 = (bf16[8,64,128]{2,1,0:T(8,128)(2,1)S(1)}, bf16[8,64,128]{2,1,0:T(8,128)(2,1)S(1)}, u32[]{:S(2)}, u32[]{:S(2)}) collective-permute-start(bf16[8,64,128]{2,1,0:T(8,128)(2,1)S(1)} %get-tuple-element.55.refs_2_.refs_3_), channel_id=1, source_target_pairs={{0,2},{1,3},{2,0},{3,1},{4,6},{5,7},{6,4},{7,5},{8,10},{9,11},{10,... | collective-permute-start | bytes 393224 | tf_op jit(solution)/shard_map/ppermute | solution.py:39
  44.0 5.2 %collective-permute-start.26 = (bf16[9,64,128]{2,1,0:T(8,128)(2,1)S(1)}, bf16[9,64,128]{2,1,0:T(8,128)(2,1)S(1)}, u32[]{:S(2)}, u32[]{:S(2)}) collective-permute-start(bf16[9,64,128]{2,1,0:T(8,128)(2,1)S(1)} %pad_maximum_fusion.1), channel_id=1, source_target_pairs={{0,8},{8,0},{16,24},{24,16},{1,9},{9,1},{17,25},{25,17},{2,10},{10... | collective-permute-start | bytes 442376 | tf_op jit(solution)/shard_map/ppermute | solution.py:39
  45.3 1.5 %collective-permute-start.20 = (bf16[8,64,128]{2,1,0:T(8,128)(2,1)S(1)}, bf16[8,64,128]{2,1,0:T(8,128)(2,1)S(1)}, u32[]{:S(2)}, u32[]{:S(2)}) collective-permute-start(bf16[8,64,128]{2,1,0:T(8,128)(2,1)S(1)} %get-tuple-element.55.refs_2_.refs_3_), channel_id=1, source_target_pairs={{0,1},{1,0},{2,3},{3,2},{4,5},{5,4},{6,7},{7,6},{8,9},{9,8},{10,11... | collective-permute-start | bytes 393224 | tf_op jit(solution)/shard_map/ppermute | solution.py:39
  45.3 1.5 %collective-permute-start.21 = (bf16[8,64,128]{2,1,0:T(8,128)(2,1)S(1)}, bf16[8,64,128]{2,1,0:T(8,128)(2,1)S(1)}, u32[]{:S(2)}, u32[]{:S(2)}) collective-permute-start(bf16[8,64,128]{2,1,0:T(8,128)(2,1)S(1)} %collective-permute-done.17.refs_3_), channel_id=1, source_target_pairs={{0,1},{1,0},{2,3},{3,2},{4,5},{5,4},{6,7},{7,6},{8,9},{9,8},{10,11... | collective-permute-start | bytes 393224 | tf_op jit(solution)/shard_map/ppermute | solution.py:39
  46.4 1.4 %collective-permute-start.23 = (bf16[8,64,128]{2,1,0:T(8,128)(2,1)S(1)}, bf16[8,64,128]{2,1,0:T(8,128)(2,1)S(1)}, u32[]{:S(2)}, u32[]{:S(2)}) collective-permute-start(bf16[8,64,128]{2,1,0:T(8,128)(2,1)S(1)} %collective-permute-done.19.refs_5_), channel_id=1, source_target_pairs={{0,1},{1,0},{2,3},{3,2},{4,5},{5,4},{6,7},{7,6},{8,9},{9,8},{10,11... | collective-permute-start | bytes 393224 | tf_op jit(solution)/shard_map/ppermute | solution.py:39
  50.6 4.6 %collective-permute-start.27 = (bf16[4,512,128]{2,1,0:T(8,128)(2,1)S(1)}, bf16[4,512,128]{2,1,0:T(8,128)(2,1)S(1)}, u32[]{:S(2)}, u32[]{:S(2)}) collective-permute-start(bf16[4,512,128]{2,1,0:T(8,128)(2,1)S(1)} %get-tuple-element.62), channel_id=1, source_target_pairs={{0,1},{1,0},{2,3},{3,2},{4,5},{5,4},{6,7},{7,6},{8,9},{9,8},{10,11... | collective-permute-start | bytes 1572872 | tf_op jit(solution)/shard_map/ppermute | solution.py:39
  50.8 7.5 %collective-permute-start.31 = (bf16[512,128]{1,0:T(8,128)(2,1)S(1)}, bf16[512,128]{1,0:T(8,128)(2,1)S(1)}, u32[]{:S(2)}, u32[]{:S(2)}) collective-permute-start(bf16[512,128]{1,0:T(8,128)(2,1)S(1)} %get-tuple-element.67), channel_id=1, source_target_pairs={{0,8},{8,0},{16,24},{24,16},{1,9},{9,1},{17,25},{25,17},{2,10},{10... | collective-permute-start | bytes 393224 | tf_op jit(solution)/shard_map/ppermute | solution.py:39
  52.5 12.9 %collective-permute-start.32 = (bf16[512,128]{1,0:T(8,128)(2,1)S(1)}, bf16[512,128]{1,0:T(8,128)(2,1)S(1)}, u32[]{:S(2)}, u32[]{:S(2)}) collective-permute-start(bf16[512,128]{1,0:T(8,128)(2,1)S(1)} %get-tuple-element.68), channel_id=1, source_target_pairs={{0,16},{8,24},{16,0},{24,8},{1,17},{9,25},{17,1},{25,9},{2,18},{10... | collective-permute-start | bytes 393224 | tf_op jit(solution)/shard_map/ppermute | solution.py:39
  53.3 12.1 %collective-permute-start.33 = (bf16[512,128]{1,0:T(8,128)(2,1)S(1)}, bf16[512,128]{1,0:T(8,128)(2,1)S(1)}, u32[]{:S(2)}, u32[]{:S(2)}) collective-permute-start(bf16[512,128]{1,0:T(8,128)(2,1)S(1)} %get-tuple-element.69), channel_id=1, source_target_pairs={{0,24},{8,16},{16,8},{24,0},{1,25},{9,17},{17,9},{25,1},{2,26},{10... | collective-permute-start | bytes 393224 | tf_op jit(solution)/shard_map/ppermute | solution.py:39
  55.3 10.1 %collective-permute-start.28 = (bf16[512,128]{1,0:T(8,128)(2,1)S(1)}, bf16[512,128]{1,0:T(8,128)(2,1)S(1)}, u32[]{:S(2)}, u32[]{:S(2)}) collective-permute-start(bf16[512,128]{1,0:T(8,128)(2,1)S(1)} %get-tuple-element.64), channel_id=1, source_target_pairs={{0,6},{1,7},{2,4},{3,5},{4,2},{5,3},{6,0},{7,1},{8,14},{9,15},{10,... | collective-permute-start | bytes 393224 | tf_op jit(solution)/shard_map/ppermute | solution.py:39
  57.8 7.6 %collective-permute-start.29 = (bf16[512,128]{1,0:T(8,128)(2,1)S(1)}, bf16[512,128]{1,0:T(8,128)(2,1)S(1)}, u32[]{:S(2)}, u32[]{:S(2)}) collective-permute-start(bf16[512,128]{1,0:T(8,128)(2,1)S(1)} %get-tuple-element.65), channel_id=1, source_target_pairs={{0,4},{1,5},{2,6},{3,7},{4,0},{5,1},{6,2},{7,3},{8,12},{9,13},{10,... | collective-permute-start | bytes 393224 | tf_op jit(solution)/shard_map/ppermute | solution.py:39
  58.3 7.1 %collective-permute-start.30 = (bf16[512,128]{1,0:T(8,128)(2,1)S(1)}, bf16[512,128]{1,0:T(8,128)(2,1)S(1)}, u32[]{:S(2)}, u32[]{:S(2)}) collective-permute-start(bf16[512,128]{1,0:T(8,128)(2,1)S(1)} %get-tuple-element.66), channel_id=1, source_target_pairs={{0,2},{1,3},{2,0},{3,1},{4,6},{5,7},{6,4},{7,5},{8,10},{9,11},{10,... | collective-permute-start | bytes 393224 | tf_op jit(solution)/shard_map/ppermute | solution.py:39
  65.6 8.7 %collective-permute-start.42 = (bf16[8,64,128]{2,1,0:T(8,128)(2,1)S(1)}, bf16[8,64,128]{2,1,0:T(8,128)(2,1)S(1)}, u32[]{:S(2)}, u32[]{:S(2)}) collective-permute-start(bf16[8,64,128]{2,1,0:T(8,128)(2,1)S(1)} %get-tuple-element.71.refs_2_.refs_3_), channel_id=1, source_target_pairs={{0,16},{8,24},{16,0},{24,8},{1,17},{9,25},{17,1},{25,9},{2,18},{10... | collective-permute-start | bytes 393224 | tf_op jit(solution)/shard_map/ppermute | solution.py:39
  68.2 5.7 %collective-permute-start.41 = (bf16[7,64,128]{2,1,0:T(8,128)(2,1)S(1)}, bf16[7,64,128]{2,1,0:T(8,128)(2,1)S(1)}, u32[]{:S(2)}, u32[]{:S(2)}) collective-permute-start(bf16[7,64,128]{2,1,0:T(8,128)(2,1)S(1)} %slice.22), channel_id=1, source_target_pairs={{0,8},{8,0},{16,24},{24,16},{1,9},{9,1},{17,25},{25,17},{2,10},{10... | collective-permute-start | bytes 344072 | tf_op jit(solution)/shard_map/ppermute | solution.py:39
  68.3 7.0 %collective-permute-start.34 = (bf16[8,64,128]{2,1,0:T(8,128)(2,1)S(1)}, bf16[8,64,128]{2,1,0:T(8,128)(2,1)S(1)}, u32[]{:S(2)}, u32[]{:S(2)}) collective-permute-start(bf16[8,64,128]{2,1,0:T(8,128)(2,1)S(1)} %get-tuple-element.71.refs_2_.refs_3_), channel_id=1, source_target_pairs={{0,6},{1,7},{2,4},{3,5},{4,2},{5,3},{6,0},{7,1},{8,14},{9,15},{10,... | collective-permute-start | bytes 393224 | tf_op jit(solution)/shard_map/ppermute | solution.py:39
  70.8 5.6 %collective-permute-start.35 = (bf16[8,64,128]{2,1,0:T(8,128)(2,1)S(1)}, bf16[8,64,128]{2,1,0:T(8,128)(2,1)S(1)}, u32[]{:S(2)}, u32[]{:S(2)}) collective-permute-start(bf16[8,64,128]{2,1,0:T(8,128)(2,1)S(1)} %get-tuple-element.71.refs_2_.refs_3_), channel_id=1, source_target_pairs={{0,4},{1,5},{2,6},{3,7},{4,0},{5,1},{6,2},{7,3},{8,12},{9,13},{10,... | collective-permute-start | bytes 393224 | tf_op jit(solution)/shard_map/ppermute | solution.py:39
  71.3 5.2 %collective-permute-start.36 = (bf16[8,64,128]{2,1,0:T(8,128)(2,1)S(1)}, bf16[8,64,128]{2,1,0:T(8,128)(2,1)S(1)}, u32[]{:S(2)}, u32[]{:S(2)}) collective-permute-start(bf16[8,64,128]{2,1,0:T(8,128)(2,1)S(1)} %get-tuple-element.71.refs_2_.refs_3_), channel_id=1, source_target_pairs={{0,2},{1,3},{2,0},{3,1},{4,6},{5,7},{6,4},{7,5},{8,10},{9,11},{10,... | collective-permute-start | bytes 393224 | tf_op jit(solution)/shard_map/ppermute | solution.py:39
  74.3 5.2 %collective-permute-start.43 = (bf16[9,64,128]{2,1,0:T(8,128)(2,1)S(1)}, bf16[9,64,128]{2,1,0:T(8,128)(2,1)S(1)}, u32[]{:S(2)}, u32[]{:S(2)}) collective-permute-start(bf16[9,64,128]{2,1,0:T(8,128)(2,1)S(1)} %pad_maximum_fusion.2), channel_id=1, source_target_pairs={{0,8},{8,0},{16,24},{24,16},{1,9},{9,1},{17,25},{25,17},{2,10},{10... | collective-permute-start | bytes 442376 | tf_op jit(solution)/shard_map/ppermute | solution.py:39
  75.2 1.7 %collective-permute-start.37 = (bf16[8,64,128]{2,1,0:T(8,128)(2,1)S(1)}, bf16[8,64,128]{2,1,0:T(8,128)(2,1)S(1)}, u32[]{:S(2)}, u32[]{:S(2)}) collective-permute-start(bf16[8,64,128]{2,1,0:T(8,128)(2,1)S(1)} %get-tuple-element.71.refs_2_.refs_3_), channel_id=1, source_target_pairs={{0,1},{1,0},{2,3},{3,2},{4,5},{5,4},{6,7},{7,6},{8,9},{9,8},{10,11... | collective-permute-start | bytes 393224 | tf_op jit(solution)/shard_map/ppermute | solution.py:39
  75.2 1.7 %collective-permute-start.38 = (bf16[8,64,128]{2,1,0:T(8,128)(2,1)S(1)}, bf16[8,64,128]{2,1,0:T(8,128)(2,1)S(1)}, u32[]{:S(2)}, u32[]{:S(2)}) collective-permute-start(bf16[8,64,128]{2,1,0:T(8,128)(2,1)S(1)} %collective-permute-done.34.refs_3_), channel_id=1, source_target_pairs={{0,1},{1,0},{2,3},{3,2},{4,5},{5,4},{6,7},{7,6},{8,9},{9,8},{10,11... | collective-permute-start | bytes 393224 | tf_op jit(solution)/shard_map/ppermute | solution.py:39
  76.5 1.4 %collective-permute-start.40 = (bf16[8,64,128]{2,1,0:T(8,128)(2,1)S(1)}, bf16[8,64,128]{2,1,0:T(8,128)(2,1)S(1)}, u32[]{:S(2)}, u32[]{:S(2)}) collective-permute-start(bf16[8,64,128]{2,1,0:T(8,128)(2,1)S(1)} %collective-permute-done.36.refs_5_), channel_id=1, source_target_pairs={{0,1},{1,0},{2,3},{3,2},{4,5},{5,4},{6,7},{7,6},{8,9},{9,8},{10,11... | collective-permute-start | bytes 393224 | tf_op jit(solution)/shard_map/ppermute | solution.py:39
  80.7 4.7 %collective-permute-start.44 = (f32[40,128]{1,0:T(8,128)S(1)}, f32[40,128]{1,0:T(8,128)S(1)}, u32[]{:S(2)}, u32[]{:S(2)}) collective-permute-start(f32[40,128]{1,0:T(8,128)S(1)} %shard_map.74), channel_id=1, source_target_pairs={{0,6},{1,7},{2,4},{3,5},{4,2},{5,3},{6,0},{7,1},{8,14},{9,15},{10,... | collective-permute-start | bytes 61448 | tf_op jit(solution)/shard_map/ppermute | solution.py:39
  82.8 3.8 %collective-permute-start.45 = (f32[40,128]{1,0:T(8,128)S(1)}, f32[40,128]{1,0:T(8,128)S(1)}, u32[]{:S(2)}, u32[]{:S(2)}) collective-permute-start(f32[40,128]{1,0:T(8,128)S(1)} %shard_map.74), channel_id=1, source_target_pairs={{0,4},{1,5},{2,6},{3,7},{4,0},{5,1},{6,2},{7,3},{8,12},{9,13},{10,... | collective-permute-start | bytes 61448 | tf_op jit(solution)/shard_map/ppermute | solution.py:39
  83.6 3.8 %collective-permute-start.46 = (f32[40,128]{1,0:T(8,128)S(1)}, f32[40,128]{1,0:T(8,128)S(1)}, u32[]{:S(2)}, u32[]{:S(2)}) collective-permute-start(f32[40,128]{1,0:T(8,128)S(1)} %shard_map.74), channel_id=1, source_target_pairs={{0,2},{1,3},{2,0},{3,1},{4,6},{5,7},{6,4},{7,5},{8,10},{9,11},{10,... | collective-permute-start | bytes 61448 | tf_op jit(solution)/shard_map/ppermute | solution.py:39
  87.4 5.6 %collective-permute-start.47 = (f32[40,128]{1,0:T(8,128)S(1)}, f32[40,128]{1,0:T(8,128)S(1)}, u32[]{:S(2)}, u32[]{:S(2)}) collective-permute-start(f32[40,128]{1,0:T(8,128)S(1)} %add_add_fusion.1), channel_id=1, source_target_pairs={{0,24},{8,16},{16,8},{24,0},{1,25},{9,17},{17,9},{25,1},{2,26},{10... | collective-permute-start | bytes 61448 | tf_op jit(solution)/shard_map/ppermute | solution.py:39
  89.3 4.9 %collective-permute-start.48 = (f32[40,128]{1,0:T(8,128)S(1)}, f32[40,128]{1,0:T(8,128)S(1)}, u32[]{:S(2)}, u32[]{:S(2)}) collective-permute-start(f32[40,128]{1,0:T(8,128)S(1)} %add_add_fusion.1), channel_id=1, source_target_pairs={{0,16},{8,24},{16,0},{24,8},{1,17},{9,25},{17,1},{25,9},{2,18},{10... | collective-permute-start | bytes 61448 | tf_op jit(solution)/shard_map/ppermute | solution.py:39
  90.2 4.0 %collective-permute-start.49 = (f32[40,128]{1,0:T(8,128)S(1)}, f32[40,128]{1,0:T(8,128)S(1)}, u32[]{:S(2)}, u32[]{:S(2)}) collective-permute-start(f32[40,128]{1,0:T(8,128)S(1)} %add_add_fusion.1), channel_id=1, source_target_pairs={{0,8},{8,0},{16,24},{24,16},{1,9},{9,1},{17,25},{25,17},{2,10},{10... | collective-permute-start | bytes 61448 | tf_op jit(solution)/shard_map/ppermute | solution.py:39
  (8 other events, 21.2 us)

commit v25 on v21

--- a/solution.py
+++ b/solution.py
@@ -433,7 +433,8 @@
         )
         parts = gather(rounded, (*first, *zeros))
         kept, swap, col_own, col_send = products(tiles, table, *parts, zeros, runs, degree)
-        col_got = exchange(col_send, "row")
+        near, *far = exchange(col_send, "row")
+        col_got = [near, *far[::-1]]
         row_own, *row_send = merge(kept, trade(swap, "col", 1), vectors_n, degree)
         row_degree = row_send[:1] if degree else []
         row_got = exchange(row_send[len(row_degree) :], "col", 2)[::-1]

time: 99.3 us -> 102 us (1.027)
  waiting for transfers between devices: 27 us -> 36.3 us
  starting transfers between devices: 54.6 us -> 47.6 us
    ppermute x51, waiting for transfers between devices: 27 us -> 36.3 us  [trade(): return lax.ppermute(part, axis, [(i, i ^ d) for i in range(n)])]
    ppermute x51, starting transfers between devices: 54.6 us -> 47.6 us  [trade(): return lax.ppermute(part, axis, [(i, i ^ d) for i in range(n)])]
  transfers between devices with their start and end apart: 51 -> 51, of which waited for: 25 -> 26; matrix products, arithmetic and copies ran while one was open for 0% -> 0% of each run, Pallas kernels for 5% -> 5%
where the time goes in v25:
time: 102 us; the launch traced here: 101 us
  starting transfers between devices  47.6 us (47%)
  waiting for transfers between devices  36.3 us (36%)
  Pallas kernels  12.9 us (13%)
  local copies, waits for them, and re-layouts  3.59 us (4%)
    ppermute x51, starting transfers between devices, trade(): return lax.ppermute(part, axis, [(i, i ^ d) for i in range(n)])  47.6 us
    ppermute x51, waiting for transfers between devices, trade(): return lax.ppermute(part, axis, [(i, i ^ d) for i in range(n)])  36.3 us
    pallas_call x17, Pallas kernels, call(): pl.pallas_call(lambda *refs: kernel(*refs[len(after):]), out_shape=jax.tr...  12.9 us
    unnamed x10, local copies, waits for them, and re-layouts  3.49 us
  transfers between devices with their start and end apart: 51, of which 26 were waited for; matrix products, arithmetic and copies ran while one was open for 0% of the time, Pallas kernels for 5%

profile of v25, /device:TPU:0, one launch (start us, length us, event | category | flops | bytes accessed | tf_op | source)
XLA Modules:
  0.0 101.4 jit_solution(4717507494607258156)
XLA Ops:
  0.6 0.9 copy-done
  1.6 4.1 %collective-permute-start.8 = (bf16[8,64,128]{2,1,0:T(8,128)(2,1)S(1)}, bf16[8,64,128]{2,1,0:T(8,128)(2,1)S(1)}, u32[]{:S(2)}, u32[]{:S(2)}) collective-permute-start(bf16[8,64,128]{2,1,0:T(8,128)(2,1)S(1)} %shard_map.61.refs_2_.refs_3_), channel_id=1, source_target_pairs={{0,16},{8,24},{16,0},{24,8},{1,17},{9,25},{17,1},{25,9},{2,18},{10... | collective-permute-start | bytes 393224 | tf_op jit(solution)/shard_map/ppermute | solution.py:39
  5.7 1.6 %collective-permute-start.7 = (bf16[7,64,128]{2,1,0:T(8,128)(2,1)S(1)}, bf16[7,64,128]{2,1,0:T(8,128)(2,1)S(1)}, u32[]{:S(2)}, u32[]{:S(2)}) collective-permute-start(bf16[7,64,128]{2,1,0:T(8,128)(2,1)S(1)} %slice.24), channel_id=1, source_target_pairs={{0,8},{8,0},{16,24},{24,16},{1,9},{9,1},{17,25},{25,17},{2,10},{10... | collective-permute-start | bytes 344072 | tf_op jit(solution)/shard_map/ppermute | solution.py:39
  7.4 2.4 %collective-permute-start = (bf16[8,64,128]{2,1,0:T(8,128)(2,1)S(1)}, bf16[8,64,128]{2,1,0:T(8,128)(2,1)S(1)}, u32[]{:S(2)}, u32[]{:S(2)}) collective-permute-start(bf16[8,64,128]{2,1,0:T(8,128)(2,1)S(1)} %shard_map.61.refs_2_.refs_3_), channel_id=1, source_target_pairs={{0,6},{1,7},{2,4},{3,5},{4,2},{5,3},{6,0},{7,1},{8,14},{9,15},{10,... | collective-permute-start | bytes 393224 | tf_op jit(solution)/shard_map/ppermute | solution.py:39
  11.0 0.7 copy-done.3
  11.7 0.7 copy-done.4
  12.6 0.9 collective-permute-start.9
  14.0 1.7 %collective-permute-done.1.refs_4_ = bf16[8,64,128]{2,1,0:T(8,128)(2,1)S(1)} collective-permute-done((bf16[8,64,128]{2,1,0:T(8,128)(2,1)S(1)}, bf16[8,64,128]{2,1,0:T(8,128)(2,1)S(1)}, u32[]{:S(2)}, u32[]{:S(2)}) %collective-permute-start.1) | collective-permute-done | bytes 131104 | tf_op jit(solution)/shard_map/ppermute | solution.py:39
  16.3 1.2 %copy-done.2 = bf16[1,1,32,128,128]{4,3,2,1,0:T(8,128)(2,1)S(1)} copy-done((bf16[1,1,32,128,128]{4,3,2,1,0:T(8,128)(2,1)S(1)}, bf16[1,1,32,128,128]{4,3,2,1,0:T(8,128)(2,1)}, u32[]{:S(2)}) %copy-start.2) | copy-done | bytes 1048600
  17.6 1.2 %shard_map.63 = (f32[8,80,128]{2,1,0:T(8,128)S(1)}, f32[32,80,128]{2,1,0:T(8,128)S(1)}, bf16[528,128]{1,0:T(8,128)(2,1)S(1)}, bf16[528,128]{1,0:T(8,128)(2,1)S(1)}, bf16[528,128]{1,0:T(8,128)(2,1)S(1)}) custom-call(s32[3,32]{1,0:T(4,128)S(1)} %shard_map.59.refs_0_.refs_1_, ...), custom_call_target="tpu_custom_call", output_to_operand_aliasing={{1}: (10, {})} | custom-call | flops 67108864 | bytes 3408256 | tf_op jit(solution)/shard_map/pallas_call | solution.py:25
  18.8 1.5 %shard_map.64 = (f32[64,80,128]{2,1,0:T(8,128)S(1)}, bf16[4,528,128]{2,1,0:T(8,128)(2,1)S(1)}) custom-call(f32[8,80,128]{2,1,0:T(8,128)S(1)} %get-tuple-element.39.refs_0_.refs_3_, s32[3,32]{1,0:T(4,128)S(1)} %shard_map.59.refs_0_.refs_1_, bf16[32,128,128]{2,1,0:T(8,128)(2,1)S(1)} %shard_map.60.refs_1_.refs_2_, ...), custom_call_target="tpu_custom_call", output_to_operand_aliasing={{0}: (7, {})} | custom-call | flops 67108864 | bytes 4194688 | tf_op jit(solution)/shard_map/pallas_call | solution.py:25
  20.9 2.5 %collective-permute-start.15 = (bf16[528,128]{1,0:T(8,128)(2,1)S(1)}, bf16[528,128]{1,0:T(8,128)(2,1)S(1)}, u32[]{:S(2)}, u32[]{:S(2)}) collective-permute-start(bf16[528,128]{1,0:T(8,128)(2,1)S(1)} %get-tuple-element.51), channel_id=1, source_target_pairs={{0,24},{8,16},{16,8},{24,0},{1,25},{9,17},{17,9},{25,1},{2,26},{10... | collective-permute-start | bytes 405512 | tf_op jit(solution)/shard_map/ppermute | solution.py:39
  24.0 2.2 %collective-permute-start.11 = (bf16[528,128]{1,0:T(8,128)(2,1)S(1)}, bf16[528,128]{1,0:T(8,128)(2,1)S(1)}, u32[]{:S(2)}, u32[]{:S(2)}) collective-permute-start(bf16[528,128]{1,0:T(8,128)(2,1)S(1)} %get-tuple-element.47), channel_id=1, source_target_pairs={{0,6},{1,7},{2,4},{3,5},{4,2},{5,3},{6,0},{7,1},{8,14},{9,15},{10,... | collective-permute-start | bytes 405512 | tf_op jit(solution)/shard_map/ppermute | solution.py:39
  26.3 0.8 collective-permute-start.12
  27.1 0.8 collective-permute-start.13
  27.9 2.8 %collective-permute-done.15.refs_8_ = bf16[528,128]{1,0:T(8,128)(2,1)S(1)} collective-permute-done((bf16[528,128]{1,0:T(8,128)(2,1)S(1)}, bf16[528,128]{1,0:T(8,128)(2,1)S(1)}, u32[]{:S(2)}, u32[]{:S(2)}) %collective-permute-start.15) | collective-permute-done | bytes 135200 | tf_op jit(solution)/shard_map/ppermute | solution.py:39
  30.7 5.5 %collective-permute-done.16.refs_9_ = bf16[528,128]{1,0:T(8,128)(2,1)S(1)} collective-permute-done((bf16[528,128]{1,0:T(8,128)(2,1)S(1)}, bf16[528,128]{1,0:T(8,128)(2,1)S(1)}, u32[]{:S(2)}, u32[]{:S(2)}) %collective-permute-start.16) | collective-permute-done | bytes 135200 | tf_op jit(solution)/shard_map/ppermute | solution.py:39
  36.5 3.2 %collective-permute-start.24 = (bf16[7,64,128]{2,1,0:T(8,128)(2,1)S(1)}, bf16[7,64,128]{2,1,0:T(8,128)(2,1)S(1)}, u32[]{:S(2)}, u32[]{:S(2)}) collective-permute-start(bf16[7,64,128]{2,1,0:T(8,128)(2,1)S(1)} %slice.20), channel_id=1, source_target_pairs={{0,8},{8,0},{16,24},{24,16},{1,9},{9,1},{17,25},{25,17},{2,10},{10... | collective-permute-start | bytes 344072 | tf_op jit(solution)/shard_map/ppermute | solution.py:39
  39.8 2.4 %collective-permute-start.17 = (bf16[8,64,128]{2,1,0:T(8,128)(2,1)S(1)}, bf16[8,64,128]{2,1,0:T(8,128)(2,1)S(1)}, u32[]{:S(2)}, u32[]{:S(2)}) collective-permute-start(bf16[8,64,128]{2,1,0:T(8,128)(2,1)S(1)} %get-tuple-element.55.refs_2_.refs_3_), channel_id=1, source_target_pairs={{0,6},{1,7},{2,4},{3,5},{4,2},{5,3},{6,0},{7,1},{8,14},{9,15},{10,... | collective-permute-start | bytes 393224 | tf_op jit(solution)/shard_map/ppermute | solution.py:39
  43.5 1.6 %collective-permute-done.24.refs_5_ = bf16[7,64,128]{2,1,0:T(8,128)(2,1)S(1)} collective-permute-done((bf16[7,64,128]{2,1,0:T(8,128)(2,1)S(1)}, bf16[7,64,128]{2,1,0:T(8,128)(2,1)S(1)}, u32[]{:S(2)}, u32[]{:S(2)}) %collective-permute-start.24) | collective-permute-done | bytes 114720 | tf_op jit(solution)/shard_map/ppermute | solution.py:39
  45.2 1.5 %collective-permute-done.17.refs_3_ = bf16[8,64,128]{2,1,0:T(8,128)(2,1)S(1)} collective-permute-done((bf16[8,64,128]{2,1,0:T(8,128)(2,1)S(1)}, bf16[8,64,128]{2,1,0:T(8,128)(2,1)S(1)}, u32[]{:S(2)}, u32[]{:S(2)}) %collective-permute-start.17) | collective-permute-done | bytes 131104 | tf_op jit(solution)/shard_map/ppermute | solution.py:39
  46.7 0.9 collective-permute-done.18.refs_4_
  48.2 0.8 collective-permute-done.22.refs_8_
  49.2 1.0 %shard_map.68 = (f32[8,64,128]{2,1,0:T(8,128)S(1)}, f32[32,64,128]{2,1,0:T(8,128)S(1)}, bf16[512,128]{1,0:T(8,128)(2,1)S(1)}, bf16[512,128]{1,0:T(8,128)(2,1)S(1)}, bf16[512,128]{1,0:T(8,128)(2,1)S(1)}) custom-call(s32[3,32]{1,0:T(4,128)S(1)} %shard_map.59.refs_0_.refs_1_, ...), custom_call_target="tpu_custom_call", output_to_operand_aliasing={{1}: (10, {})} | custom-call | flops 67108864 | bytes 3146112 | tf_op jit(solution)/shard_map/pallas_call | solution.py:25
  50.8 1.4 %shard_map.69 = (f32[64,64,128]{2,1,0:T(8,128)S(1)}, bf16[4,512,128]{2,1,0:T(8,128)(2,1)S(1)}) custom-call(f32[8,64,128]{2,1,0:T(8,128)S(1)} %get-tuple-element.57.refs_0_.refs_4_, s32[3,32]{1,0:T(4,128)S(1)} %shard_map.59.refs_0_.refs_1_, bf16[32,128,128]{2,1,0:T(8,128)(2,1)S(1)} %shard_map.60.refs_1_.refs_2_, ...), custom_call_target="tpu_custom_call", output_to_operand_aliasing={{0}: (7, {})} | custom-call | flops 67108864 | bytes 3670400 | tf_op jit(solution)/shard_map/pallas_call | solution.py:25
  52.7 1.2 %collective-permute-start.32 = (bf16[512,128]{1,0:T(8,128)(2,1)S(1)}, bf16[512,128]{1,0:T(8,128)(2,1)S(1)}, u32[]{:S(2)}, u32[]{:S(2)}) collective-permute-start(bf16[512,128]{1,0:T(8,128)(2,1)S(1)} %get-tuple-element.68), channel_id=1, source_target_pairs={{0,24},{8,16},{16,8},{24,0},{1,25},{9,17},{17,9},{25,1},{2,26},{10... | collective-permute-start | bytes 393224 | tf_op jit(solution)/shard_map/ppermute | solution.py:39
  53.9 2.0 %collective-permute-start.33 = (bf16[512,128]{1,0:T(8,128)(2,1)S(1)}, bf16[512,128]{1,0:T(8,128)(2,1)S(1)}, u32[]{:S(2)}, u32[]{:S(2)}) collective-permute-start(bf16[512,128]{1,0:T(8,128)(2,1)S(1)} %get-tuple-element.69), channel_id=1, source_target_pairs={{0,16},{8,24},{16,0},{24,8},{1,17},{9,25},{17,1},{25,9},{2,18},{10... | collective-permute-start | bytes 393224 | tf_op jit(solution)/shard_map/ppermute | solution.py:39
  56.0 2.6 %collective-permute-start.28 = (bf16[512,128]{1,0:T(8,128)(2,1)S(1)}, bf16[512,128]{1,0:T(8,128)(2,1)S(1)}, u32[]{:S(2)}, u32[]{:S(2)}) collective-permute-start(bf16[512,128]{1,0:T(8,128)(2,1)S(1)} %get-tuple-element.64), channel_id=1, source_target_pairs={{0,6},{1,7},{2,4},{3,5},{4,2},{5,3},{6,0},{7,1},{8,14},{9,15},{10,... | collective-permute-start | bytes 393224 | tf_op jit(solution)/shard_map/ppermute | solution.py:39
  59.0 2.0 %collective-permute-done.31.refs_8_ = bf16[512,128]{1,0:T(8,128)(2,1)S(1)} collective-permute-done((bf16[512,128]{1,0:T(8,128)(2,1)S(1)}, bf16[512,128]{1,0:T(8,128)(2,1)S(1)}, u32[]{:S(2)}, u32[]{:S(2)}) %collective-permute-start.31) | collective-permute-done | bytes 131104 | tf_op jit(solution)/shard_map/ppermute | solution.py:39
  61.1 1.5 %collective-permute-start.30 = (bf16[512,128]{1,0:T(8,128)(2,1)S(1)}, bf16[512,128]{1,0:T(8,128)(2,1)S(1)}, u32[]{:S(2)}, u32[]{:S(2)}) collective-permute-start(bf16[512,128]{1,0:T(8,128)(2,1)S(1)} %get-tuple-element.66), channel_id=1, source_target_pairs={{0,2},{1,3},{2,0},{3,1},{4,6},{5,7},{6,4},{7,5},{8,10},{9,11},{10,... | collective-permute-start | bytes 393224 | tf_op jit(solution)/shard_map/ppermute | solution.py:39
  62.6 5.3 %collective-permute-done.33.refs_10_ = bf16[512,128]{1,0:T(8,128)(2,1)S(1)} collective-permute-done((bf16[512,128]{1,0:T(8,128)(2,1)S(1)}, bf16[512,128]{1,0:T(8,128)(2,1)S(1)}, u32[]{:S(2)}, u32[]{:S(2)}) %collective-permute-start.33) | collective-permute-done | bytes 131104 | tf_op jit(solution)/shard_map/ppermute | solution.py:39
  68.2 1.8 %collective-permute-start.41 = (bf16[7,64,128]{2,1,0:T(8,128)(2,1)S(1)}, bf16[7,64,128]{2,1,0:T(8,128)(2,1)S(1)}, u32[]{:S(2)}, u32[]{:S(2)}) collective-permute-start(bf16[7,64,128]{2,1,0:T(8,128)(2,1)S(1)} %slice.22), channel_id=1, source_target_pairs={{0,8},{8,0},{16,24},{24,16},{1,9},{9,1},{17,25},{25,17},{2,10},{10... | collective-permute-start | bytes 344072 | tf_op jit(solution)/shard_map/ppermute | solution.py:39
  70.0 2.8 %collective-permute-start.34 = (bf16[8,64,128]{2,1,0:T(8,128)(2,1)S(1)}, bf16[8,64,128]{2,1,0:T(8,128)(2,1)S(1)}, u32[]{:S(2)}, u32[]{:S(2)}) collective-permute-start(bf16[8,64,128]{2,1,0:T(8,128)(2,1)S(1)} %get-tuple-element.71.refs_2_.refs_3_), channel_id=1, source_target_pairs={{0,6},{1,7},{2,4},{3,5},{4,2},{5,3},{6,0},{7,1},{8,14},{9,15},{10,... | collective-permute-start | bytes 393224 | tf_op jit(solution)/shard_map/ppermute | solution.py:39
  74.1 1.7 %collective-permute-done.41.refs_5_ = bf16[7,64,128]{2,1,0:T(8,128)(2,1)S(1)} collective-permute-done((bf16[7,64,128]{2,1,0:T(8,128)(2,1)S(1)}, bf16[7,64,128]{2,1,0:T(8,128)(2,1)S(1)}, u32[]{:S(2)}, u32[]{:S(2)}) %collective-permute-start.41) | collective-permute-done | bytes 114720 | tf_op jit(solution)/shard_map/ppermute | solution.py:39
  76.0 0.8 collective-permute-done.34.refs_3_
  76.7 1.3 %collective-permute-done.35.refs_4_ = bf16[8,64,128]{2,1,0:T(8,128)(2,1)S(1)} collective-permute-done((bf16[8,64,128]{2,1,0:T(8,128)(2,1)S(1)}, bf16[8,64,128]{2,1,0:T(8,128)(2,1)S(1)}, u32[]{:S(2)}, u32[]{:S(2)}) %collective-permute-start.35) | collective-permute-done | bytes 131104 | tf_op jit(solution)/shard_map/ppermute | solution.py:39
  78.6 0.8 collective-permute-done.39.refs_8_
  79.6 1.0 shard_map.72.refs_1_
  81.0 1.2 %shard_map.74 = f32[40,128]{1,0:T(8,128)S(1)} custom-call(s32[3,32]{1,0:T(4,128)S(1)} %shard_map.59.refs_0_.refs_1_, bf16[64,4096]{1,0:T(8,128)(2,1)S(1)} %shard_map.72.refs_1_, f32[64,128]{1,0:T(8,128)S(1)} %shard_map.73.refs_2_, bf16[8,64,128]{2,1,0:T(8,128)(2,1)S(1)} %get-tuple-element.71.refs_2_.refs_3_, ...), custom_call_target="tpu_custom_call" | custom-call | flops 33554432 | bytes 1081728 | tf_op jit(solution)/shard_map/pallas_call | solution.py:25
  82.3 1.2 %collective-permute-done.44 = f32[40,128]{1,0:T(8,128)S(1)} collective-permute-done((f32[40,128]{1,0:T(8,128)S(1)}, f32[40,128]{1,0:T(8,128)S(1)}, u32[]{:S(2)}, u32[]{:S(2)}) %collective-permute-start.44) | collective-permute-done | bytes 20512 | tf_op jit(solution)/shard_map/ppermute | solution.py:39
  83.5 2.7 %collective-permute-start.45 = (f32[40,128]{1,0:T(8,128)S(1)}, f32[40,128]{1,0:T(8,128)S(1)}, u32[]{:S(2)}, u32[]{:S(2)}) collective-permute-start(f32[40,128]{1,0:T(8,128)S(1)} %add.12), channel_id=1, source_target_pairs={{0,6},{1,7},{2,4},{3,5},{4,2},{5,3},{6,0},{7,1},{8,14},{9,15},{10,... | collective-permute-start | bytes 61448 | tf_op jit(solution)/shard_map/ppermute | solution.py:39
  87.0 1.2 %collective-permute-done.45 = f32[40,128]{1,0:T(8,128)S(1)} collective-permute-done((f32[40,128]{1,0:T(8,128)S(1)}, f32[40,128]{1,0:T(8,128)S(1)}, u32[]{:S(2)}, u32[]{:S(2)}) %collective-permute-start.45) | collective-permute-done | bytes 20512 | tf_op jit(solution)/shard_map/ppermute | solution.py:39
  88.2 1.8 %collective-permute-done.46 = f32[40,128]{1,0:T(8,128)S(1)} collective-permute-done((f32[40,128]{1,0:T(8,128)S(1)}, f32[40,128]{1,0:T(8,128)S(1)}, u32[]{:S(2)}, u32[]{:S(2)}) %collective-permute-start.46) | collective-permute-done | bytes 20512 | tf_op jit(solution)/shard_map/ppermute | solution.py:39
  90.2 2.8 %collective-permute-start.48 = (f32[40,128]{1,0:T(8,128)S(1)}, f32[40,128]{1,0:T(8,128)S(1)}, u32[]{:S(2)}, u32[]{:S(2)}) collective-permute-start(f32[40,128]{1,0:T(8,128)S(1)} %add_add_fusion.refs_1_), channel_id=1, source_target_pairs={{0,24},{8,16},{16,8},{24,0},{1,25},{9,17},{17,9},{25,1},{2,26},{10... | collective-permute-start | bytes 61448 | tf_op jit(solution)/shard_map/ppermute | solution.py:39
  93.0 1.7 %collective-permute-start.50 = (f32[40,128]{1,0:T(8,128)S(1)}, f32[40,128]{1,0:T(8,128)S(1)}, u32[]{:S(2)}, u32[]{:S(2)}) collective-permute-start(f32[40,128]{1,0:T(8,128)S(1)} %add_add_fusion.refs_1_), channel_id=1, source_target_pairs={{0,8},{8,0},{16,24},{24,16},{1,9},{9,1},{17,25},{25,17},{2,10},{10... | collective-permute-start | bytes 61448 | tf_op jit(solution)/shard_map/ppermute | solution.py:39
  94.7 1.2 %collective-permute-done.48.refs_2_ = f32[40,128]{1,0:T(8,128)S(1)} collective-permute-done((f32[40,128]{1,0:T(8,128)S(1)}, f32[40,128]{1,0:T(8,128)S(1)}, u32[]{:S(2)}, u32[]{:S(2)}) %collective-permute-start.48) | collective-permute-done | bytes 20512 | tf_op jit(solution)/shard_map/ppermute | solution.py:39
  95.9 1.8 %collective-permute-done.49.refs_3_ = f32[40,128]{1,0:T(8,128)S(1)} collective-permute-done((f32[40,128]{1,0:T(8,128)S(1)}, f32[40,128]{1,0:T(8,128)S(1)}, u32[]{:S(2)}, u32[]{:S(2)}) %collective-permute-start.49) | collective-permute-done | bytes 20512 | tf_op jit(solution)/shard_map/ppermute | solution.py:39
  97.7 3.8 %shard_map.75 = (f32[64,1024]{1,0:T(8,128)}, f32[64,64]{1,0:T(8,128)}) custom-call(f32[64,1024]{1,0:T(8,128)S(1)} %get-tuple-element.70.refs_0_, f32[40,128]{1,0:T(8,128)S(1)} %add_add_fusion.refs_1_, f32[40,128]{1,0:T(8,128)S(1)} %collective-permute-done.48.refs_2_, f32[40,128]{1,0:T(8,128)S(1)} %collective-permute-done.49.refs_3_, ...), custom_call_target="tpu_custom_call" | custom-call | bytes 344064 | tf_op jit(solution)/shard_map/pallas_call | solution.py:25
  (94 shorter events, 12.0 us)
Async XLA Ops:
  1.6 11.0 %collective-permute-start.8 = (bf16[8,64,128]{2,1,0:T(8,128)(2,1)S(1)}, bf16[8,64,128]{2,1,0:T(8,128)(2,1)S(1)}, u32[]{:S(2)}, u32[]{:S(2)}) collective-permute-start(bf16[8,64,128]{2,1,0:T(8,128)(2,1)S(1)} %shard_map.61.refs_2_.refs_3_), channel_id=1, source_target_pairs={{0,16},{8,24},{16,0},{24,8},{1,17},{9,25},{17,1},{25,9},{2,18},{10... | collective-permute-start | bytes 393224 | tf_op jit(solution)/shard_map/ppermute | solution.py:39
  5.7 6.9 %collective-permute-start.7 = (bf16[7,64,128]{2,1,0:T(8,128)(2,1)S(1)}, bf16[7,64,128]{2,1,0:T(8,128)(2,1)S(1)}, u32[]{:S(2)}, u32[]{:S(2)}) collective-permute-start(bf16[7,64,128]{2,1,0:T(8,128)(2,1)S(1)} %slice.24), channel_id=1, source_target_pairs={{0,8},{8,0},{16,24},{24,16},{1,9},{9,1},{17,25},{25,17},{2,10},{10... | collective-permute-start | bytes 344072 | tf_op jit(solution)/shard_map/ppermute | solution.py:39
  7.4 6.6 %collective-permute-start = (bf16[8,64,128]{2,1,0:T(8,128)(2,1)S(1)}, bf16[8,64,128]{2,1,0:T(8,128)(2,1)S(1)}, u32[]{:S(2)}, u32[]{:S(2)}) collective-permute-start(bf16[8,64,128]{2,1,0:T(8,128)(2,1)S(1)} %shard_map.61.refs_2_.refs_3_), channel_id=1, source_target_pairs={{0,6},{1,7},{2,4},{3,5},{4,2},{5,3},{6,0},{7,1},{8,14},{9,15},{10,... | collective-permute-start | bytes 393224 | tf_op jit(solution)/shard_map/ppermute | solution.py:39
  9.8 5.9 %collective-permute-start.1 = (bf16[8,64,128]{2,1,0:T(8,128)(2,1)S(1)}, bf16[8,64,128]{2,1,0:T(8,128)(2,1)S(1)}, u32[]{:S(2)}, u32[]{:S(2)}) collective-permute-start(bf16[8,64,128]{2,1,0:T(8,128)(2,1)S(1)} %shard_map.61.refs_2_.refs_3_), channel_id=1, source_target_pairs={{0,4},{1,5},{2,6},{3,7},{4,0},{5,1},{6,2},{7,3},{8,12},{9,13},{10,... | collective-permute-start | bytes 393224 | tf_op jit(solution)/shard_map/ppermute | solution.py:39
  10.3 5.5 %collective-permute-start.2 = (bf16[8,64,128]{2,1,0:T(8,128)(2,1)S(1)}, bf16[8,64,128]{2,1,0:T(8,128)(2,1)S(1)}, u32[]{:S(2)}, u32[]{:S(2)}) collective-permute-start(bf16[8,64,128]{2,1,0:T(8,128)(2,1)S(1)} %shard_map.61.refs_2_.refs_3_), channel_id=1, source_target_pairs={{0,2},{1,3},{2,0},{3,1},{4,6},{5,7},{6,4},{7,5},{8,10},{9,11},{10,... | collective-permute-start | bytes 393224 | tf_op jit(solution)/shard_map/ppermute | solution.py:39
  12.6 6.1 %collective-permute-start.9 = (bf16[9,64,128]{2,1,0:T(8,128)(2,1)S(1)}, bf16[9,64,128]{2,1,0:T(8,128)(2,1)S(1)}, u32[]{:S(2)}, u32[]{:S(2)}) collective-permute-start(bf16[9,64,128]{2,1,0:T(8,128)(2,1)S(1)} %pad_maximum_fusion), channel_id=1, source_target_pairs={{0,8},{8,0},{16,24},{24,16},{1,9},{9,1},{17,25},{25,17},{2,10},{10... | collective-permute-start | bytes 442376 | tf_op jit(solution)/shard_map/ppermute | solution.py:39
  13.5 4.1 %collective-permute-start.3 = (bf16[8,64,128]{2,1,0:T(8,128)(2,1)S(1)}, bf16[8,64,128]{2,1,0:T(8,128)(2,1)S(1)}, u32[]{:S(2)}, u32[]{:S(2)}) collective-permute-start(bf16[8,64,128]{2,1,0:T(8,128)(2,1)S(1)} %shard_map.61.refs_2_.refs_3_), channel_id=1, source_target_pairs={{0,1},{1,0},{2,3},{3,2},{4,5},{5,4},{6,7},{7,6},{8,9},{9,8},{10,11... | collective-permute-start | bytes 393224 | tf_op jit(solution)/shard_map/ppermute | solution.py:39
  13.9 3.7 %collective-permute-start.4 = (bf16[8,64,128]{2,1,0:T(8,128)(2,1)S(1)}, bf16[8,64,128]{2,1,0:T(8,128)(2,1)S(1)}, u32[]{:S(2)}, u32[]{:S(2)}) collective-permute-start(bf16[8,64,128]{2,1,0:T(8,128)(2,1)S(1)} %collective-permute-done.refs_3_), channel_id=1, source_target_pairs={{0,1},{1,0},{2,3},{3,2},{4,5},{5,4},{6,7},{7,6},{8,9},{9,8},{10,11... | collective-permute-start | bytes 393224 | tf_op jit(solution)/shard_map/ppermute | solution.py:39
  15.7 1.8 %collective-permute-start.5 = (bf16[8,64,128]{2,1,0:T(8,128)(2,1)S(1)}, bf16[8,64,128]{2,1,0:T(8,128)(2,1)S(1)}, u32[]{:S(2)}, u32[]{:S(2)}) collective-permute-start(bf16[8,64,128]{2,1,0:T(8,128)(2,1)S(1)} %collective-permute-done.1.refs_4_), channel_id=1, source_target_pairs={{0,1},{1,0},{2,3},{3,2},{4,5},{5,4},{6,7},{7,6},{8,9},{9,8},{10,11... | collective-permute-start | bytes 393224 | tf_op jit(solution)/shard_map/ppermute | solution.py:39
  15.8 1.8 %collective-permute-start.6 = (bf16[8,64,128]{2,1,0:T(8,128)(2,1)S(1)}, bf16[8,64,128]{2,1,0:T(8,128)(2,1)S(1)}, u32[]{:S(2)}, u32[]{:S(2)}) collective-permute-start(bf16[8,64,128]{2,1,0:T(8,128)(2,1)S(1)} %collective-permute-done.2.refs_5_), channel_id=1, source_target_pairs={{0,1},{1,0},{2,3},{3,2},{4,5},{5,4},{6,7},{7,6},{8,9},{9,8},{10,11... | collective-permute-start | bytes 393224 | tf_op jit(solution)/shard_map/ppermute | solution.py:39
  20.3 3.6 %collective-permute-start.10 = (bf16[4,528,128]{2,1,0:T(8,128)(2,1)S(1)}, bf16[4,528,128]{2,1,0:T(8,128)(2,1)S(1)}, u32[]{:S(2)}, u32[]{:S(2)}) collective-permute-start(bf16[4,528,128]{2,1,0:T(8,128)(2,1)S(1)} %get-tuple-element.44), channel_id=1, source_target_pairs={{0,1},{1,0},{2,3},{3,2},{4,5},{5,4},{6,7},{7,6},{8,9},{9,8},{10,11... | collective-permute-start | bytes 1622024 | tf_op jit(solution)/shard_map/ppermute | solution.py:39
  20.4 6.7 %collective-permute-start.14 = (bf16[528,128]{1,0:T(8,128)(2,1)S(1)}, bf16[528,128]{1,0:T(8,128)(2,1)S(1)}, u32[]{:S(2)}, u32[]{:S(2)}) collective-permute-start(bf16[528,128]{1,0:T(8,128)(2,1)S(1)} %get-tuple-element.50), channel_id=1, source_target_pairs={{0,8},{8,0},{16,24},{24,16},{1,9},{9,1},{17,25},{25,17},{2,10},{10... | collective-permute-start | bytes 405512 | tf_op jit(solution)/shard_map/ppermute | solution.py:39
  20.9 9.8 %collective-permute-start.15 = (bf16[528,128]{1,0:T(8,128)(2,1)S(1)}, bf16[528,128]{1,0:T(8,128)(2,1)S(1)}, u32[]{:S(2)}, u32[]{:S(2)}) collective-permute-start(bf16[528,128]{1,0:T(8,128)(2,1)S(1)} %get-tuple-element.51), channel_id=1, source_target_pairs={{0,24},{8,16},{16,8},{24,0},{1,25},{9,17},{17,9},{25,1},{2,26},{10... | collective-permute-start | bytes 405512 | tf_op jit(solution)/shard_map/ppermute | solution.py:39
  23.3 12.9 %collective-permute-start.16 = (bf16[528,128]{1,0:T(8,128)(2,1)S(1)}, bf16[528,128]{1,0:T(8,128)(2,1)S(1)}, u32[]{:S(2)}, u32[]{:S(2)}) collective-permute-start(bf16[528,128]{1,0:T(8,128)(2,1)S(1)} %get-tuple-element.52), channel_id=1, source_target_pairs={{0,16},{8,24},{16,0},{24,8},{1,17},{9,25},{17,1},{25,9},{2,18},{10... | collective-permute-start | bytes 405512 | tf_op jit(solution)/shard_map/ppermute | solution.py:39
  24.0 12.2 %collective-permute-start.11 = (bf16[528,128]{1,0:T(8,128)(2,1)S(1)}, bf16[528,128]{1,0:T(8,128)(2,1)S(1)}, u32[]{:S(2)}, u32[]{:S(2)}) collective-permute-start(bf16[528,128]{1,0:T(8,128)(2,1)S(1)} %get-tuple-element.47), channel_id=1, source_target_pairs={{0,6},{1,7},{2,4},{3,5},{4,2},{5,3},{6,0},{7,1},{8,14},{9,15},{10,... | collective-permute-start | bytes 405512 | tf_op jit(solution)/shard_map/ppermute | solution.py:39
  26.3 10.0 %collective-permute-start.12 = (bf16[528,128]{1,0:T(8,128)(2,1)S(1)}, bf16[528,128]{1,0:T(8,128)(2,1)S(1)}, u32[]{:S(2)}, u32[]{:S(2)}) collective-permute-start(bf16[528,128]{1,0:T(8,128)(2,1)S(1)} %get-tuple-element.48), channel_id=1, source_target_pairs={{0,4},{1,5},{2,6},{3,7},{4,0},{5,1},{6,2},{7,3},{8,12},{9,13},{10,... | collective-permute-start | bytes 405512 | tf_op jit(solution)/shard_map/ppermute | solution.py:39
  27.1 9.1 %collective-permute-start.13 = (bf16[528,128]{1,0:T(8,128)(2,1)S(1)}, bf16[528,128]{1,0:T(8,128)(2,1)S(1)}, u32[]{:S(2)}, u32[]{:S(2)}) collective-permute-start(bf16[528,128]{1,0:T(8,128)(2,1)S(1)} %get-tuple-element.49), channel_id=1, source_target_pairs={{0,2},{1,3},{2,0},{3,1},{4,6},{5,7},{6,4},{7,5},{8,10},{9,11},{10,... | collective-permute-start | bytes 405512 | tf_op jit(solution)/shard_map/ppermute | solution.py:39
  36.4 8.6 %collective-permute-start.25 = (bf16[8,64,128]{2,1,0:T(8,128)(2,1)S(1)}, bf16[8,64,128]{2,1,0:T(8,128)(2,1)S(1)}, u32[]{:S(2)}, u32[]{:S(2)}) collective-permute-start(bf16[8,64,128]{2,1,0:T(8,128)(2,1)S(1)} %get-tuple-element.55.refs_2_.refs_3_), channel_id=1, source_target_pairs={{0,16},{8,24},{16,0},{24,8},{1,17},{9,25},{17,1},{25,9},{2,18},{10... | collective-permute-start | bytes 393224 | tf_op jit(solution)/shard_map/ppermute | solution.py:39
  36.5 8.5 %collective-permute-start.24 = (bf16[7,64,128]{2,1,0:T(8,128)(2,1)S(1)}, bf16[7,64,128]{2,1,0:T(8,128)(2,1)S(1)}, u32[]{:S(2)}, u32[]{:S(2)}) collective-permute-start(bf16[7,64,128]{2,1,0:T(8,128)(2,1)S(1)} %slice.20), channel_id=1, source_target_pairs={{0,8},{8,0},{16,24},{24,16},{1,9},{9,1},{17,25},{25,17},{2,10},{10... | collective-permute-start | bytes 344072 | tf_op jit(solution)/shard_map/ppermute | solution.py:39
  39.8 6.9 %collective-permute-start.17 = (bf16[8,64,128]{2,1,0:T(8,128)(2,1)S(1)}, bf16[8,64,128]{2,1,0:T(8,128)(2,1)S(1)}, u32[]{:S(2)}, u32[]{:S(2)}) collective-permute-start(bf16[8,64,128]{2,1,0:T(8,128)(2,1)S(1)} %get-tuple-element.55.refs_2_.refs_3_), channel_id=1, source_target_pairs={{0,6},{1,7},{2,4},{3,5},{4,2},{5,3},{6,0},{7,1},{8,14},{9,15},{10,... | collective-permute-start | bytes 393224 | tf_op jit(solution)/shard_map/ppermute | solution.py:39
  42.2 5.4 %collective-permute-start.18 = (bf16[8,64,128]{2,1,0:T(8,128)(2,1)S(1)}, bf16[8,64,128]{2,1,0:T(8,128)(2,1)S(1)}, u32[]{:S(2)}, u32[]{:S(2)}) collective-permute-start(bf16[8,64,128]{2,1,0:T(8,128)(2,1)S(1)} %get-tuple-element.55.refs_2_.refs_3_), channel_id=1, source_target_pairs={{0,4},{1,5},{2,6},{3,7},{4,0},{5,1},{6,2},{7,3},{8,12},{9,13},{10,... | collective-permute-start | bytes 393224 | tf_op jit(solution)/shard_map/ppermute | solution.py:39
  42.7 5.0 %collective-permute-start.19 = (bf16[8,64,128]{2,1,0:T(8,128)(2,1)S(1)}, bf16[8,64,128]{2,1,0:T(8,128)(2,1)S(1)}, u32[]{:S(2)}, u32[]{:S(2)}) collective-permute-start(bf16[8,64,128]{2,1,0:T(8,128)(2,1)S(1)} %get-tuple-element.55.refs_2_.refs_3_), channel_id=1, source_target_pairs={{0,2},{1,3},{2,0},{3,1},{4,6},{5,7},{6,4},{7,5},{8,10},{9,11},{10,... | collective-permute-start | bytes 393224 | tf_op jit(solution)/shard_map/ppermute | solution.py:39
  45.1 5.7 %collective-permute-start.26 = (bf16[9,64,128]{2,1,0:T(8,128)(2,1)S(1)}, bf16[9,64,128]{2,1,0:T(8,128)(2,1)S(1)}, u32[]{:S(2)}, u32[]{:S(2)}) collective-permute-start(bf16[9,64,128]{2,1,0:T(8,128)(2,1)S(1)} %pad_maximum_fusion.1), channel_id=1, source_target_pairs={{0,8},{8,0},{16,24},{24,16},{1,9},{9,1},{17,25},{25,17},{2,10},{10... | collective-permute-start | bytes 442376 | tf_op jit(solution)/shard_map/ppermute | solution.py:39
  45.2 3.0 %collective-permute-start.20 = (bf16[8,64,128]{2,1,0:T(8,128)(2,1)S(1)}, bf16[8,64,128]{2,1,0:T(8,128)(2,1)S(1)}, u32[]{:S(2)}, u32[]{:S(2)}) collective-permute-start(bf16[8,64,128]{2,1,0:T(8,128)(2,1)S(1)} %get-tuple-element.55.refs_2_.refs_3_), channel_id=1, source_target_pairs={{0,1},{1,0},{2,3},{3,2},{4,5},{5,4},{6,7},{7,6},{8,9},{9,8},{10,11... | collective-permute-start | bytes 393224 | tf_op jit(solution)/shard_map/ppermute | solution.py:39
  46.7 1.5 %collective-permute-start.21 = (bf16[8,64,128]{2,1,0:T(8,128)(2,1)S(1)}, bf16[8,64,128]{2,1,0:T(8,128)(2,1)S(1)}, u32[]{:S(2)}, u32[]{:S(2)}) collective-permute-start(bf16[8,64,128]{2,1,0:T(8,128)(2,1)S(1)} %collective-permute-done.17.refs_3_), channel_id=1, source_target_pairs={{0,1},{1,0},{2,3},{3,2},{4,5},{5,4},{6,7},{7,6},{8,9},{9,8},{10,11... | collective-permute-start | bytes 393224 | tf_op jit(solution)/shard_map/ppermute | solution.py:39
  47.8 1.4 %collective-permute-start.23 = (bf16[8,64,128]{2,1,0:T(8,128)(2,1)S(1)}, bf16[8,64,128]{2,1,0:T(8,128)(2,1)S(1)}, u32[]{:S(2)}, u32[]{:S(2)}) collective-permute-start(bf16[8,64,128]{2,1,0:T(8,128)(2,1)S(1)} %collective-permute-done.19.refs_5_), channel_id=1, source_target_pairs={{0,1},{1,0},{2,3},{3,2},{4,5},{5,4},{6,7},{7,6},{8,9},{9,8},{10,11... | collective-permute-start | bytes 393224 | tf_op jit(solution)/shard_map/ppermute | solution.py:39
  52.3 3.6 %collective-permute-start.27 = (bf16[4,512,128]{2,1,0:T(8,128)(2,1)S(1)}, bf16[4,512,128]{2,1,0:T(8,128)(2,1)S(1)}, u32[]{:S(2)}, u32[]{:S(2)}) collective-permute-start(bf16[4,512,128]{2,1,0:T(8,128)(2,1)S(1)} %get-tuple-element.62), channel_id=1, source_target_pairs={{0,1},{1,0},{2,3},{3,2},{4,5},{5,4},{6,7},{7,6},{8,9},{9,8},{10,11... | collective-permute-start | bytes 1572872 | tf_op jit(solution)/shard_map/ppermute | solution.py:39
  52.3 8.7 %collective-permute-start.31 = (bf16[512,128]{1,0:T(8,128)(2,1)S(1)}, bf16[512,128]{1,0:T(8,128)(2,1)S(1)}, u32[]{:S(2)}, u32[]{:S(2)}) collective-permute-start(bf16[512,128]{1,0:T(8,128)(2,1)S(1)} %get-tuple-element.67), channel_id=1, source_target_pairs={{0,8},{8,0},{16,24},{24,16},{1,9},{9,1},{17,25},{25,17},{2,10},{10... | collective-permute-start | bytes 393224 | tf_op jit(solution)/shard_map/ppermute | solution.py:39
  52.7 9.9 %collective-permute-start.32 = (bf16[512,128]{1,0:T(8,128)(2,1)S(1)}, bf16[512,128]{1,0:T(8,128)(2,1)S(1)}, u32[]{:S(2)}, u32[]{:S(2)}) collective-permute-start(bf16[512,128]{1,0:T(8,128)(2,1)S(1)} %get-tuple-element.68), channel_id=1, source_target_pairs={{0,24},{8,16},{16,8},{24,0},{1,25},{9,17},{17,9},{25,1},{2,26},{10... | collective-permute-start | bytes 393224 | tf_op jit(solution)/shard_map/ppermute | solution.py:39
  53.9 14.0 %collective-permute-start.33 = (bf16[512,128]{1,0:T(8,128)(2,1)S(1)}, bf16[512,128]{1,0:T(8,128)(2,1)S(1)}, u32[]{:S(2)}, u32[]{:S(2)}) collective-permute-start(bf16[512,128]{1,0:T(8,128)(2,1)S(1)} %get-tuple-element.69), channel_id=1, source_target_pairs={{0,16},{8,24},{16,0},{24,8},{1,17},{9,25},{17,1},{25,9},{2,18},{10... | collective-permute-start | bytes 393224 | tf_op jit(solution)/shard_map/ppermute | solution.py:39
  56.0 11.9 %collective-permute-start.28 = (bf16[512,128]{1,0:T(8,128)(2,1)S(1)}, bf16[512,128]{1,0:T(8,128)(2,1)S(1)}, u32[]{:S(2)}, u32[]{:S(2)}) collective-permute-start(bf16[512,128]{1,0:T(8,128)(2,1)S(1)} %get-tuple-element.64), channel_id=1, source_target_pairs={{0,6},{1,7},{2,4},{3,5},{4,2},{5,3},{6,0},{7,1},{8,14},{9,15},{10,... | collective-permute-start | bytes 393224 | tf_op jit(solution)/shard_map/ppermute | solution.py:39
  58.6 9.3 %collective-permute-start.29 = (bf16[512,128]{1,0:T(8,128)(2,1)S(1)}, bf16[512,128]{1,0:T(8,128)(2,1)S(1)}, u32[]{:S(2)}, u32[]{:S(2)}) collective-permute-start(bf16[512,128]{1,0:T(8,128)(2,1)S(1)} %get-tuple-element.65), channel_id=1, source_target_pairs={{0,4},{1,5},{2,6},{3,7},{4,0},{5,1},{6,2},{7,3},{8,12},{9,13},{10,... | collective-permute-start | bytes 393224 | tf_op jit(solution)/shard_map/ppermute | solution.py:39
  61.1 6.8 %collective-permute-start.30 = (bf16[512,128]{1,0:T(8,128)(2,1)S(1)}, bf16[512,128]{1,0:T(8,128)(2,1)S(1)}, u32[]{:S(2)}, u32[]{:S(2)}) collective-permute-start(bf16[512,128]{1,0:T(8,128)(2,1)S(1)} %get-tuple-element.66), channel_id=1, source_target_pairs={{0,2},{1,3},{2,0},{3,1},{4,6},{5,7},{6,4},{7,5},{8,10},{9,11},{10,... | collective-permute-start | bytes 393224 | tf_op jit(solution)/shard_map/ppermute | solution.py:39
  68.1 7.7 %collective-permute-start.42 = (bf16[8,64,128]{2,1,0:T(8,128)(2,1)S(1)}, bf16[8,64,128]{2,1,0:T(8,128)(2,1)S(1)}, u32[]{:S(2)}, u32[]{:S(2)}) collective-permute-start(bf16[8,64,128]{2,1,0:T(8,128)(2,1)S(1)} %get-tuple-element.71.refs_2_.refs_3_), channel_id=1, source_target_pairs={{0,16},{8,24},{16,0},{24,8},{1,17},{9,25},{17,1},{25,9},{2,18},{10... | collective-permute-start | bytes 393224 | tf_op jit(solution)/shard_map/ppermute | solution.py:39
  68.2 7.6 %collective-permute-start.41 = (bf16[7,64,128]{2,1,0:T(8,128)(2,1)S(1)}, bf16[7,64,128]{2,1,0:T(8,128)(2,1)S(1)}, u32[]{:S(2)}, u32[]{:S(2)}) collective-permute-start(bf16[7,64,128]{2,1,0:T(8,128)(2,1)S(1)} %slice.22), channel_id=1, source_target_pairs={{0,8},{8,0},{16,24},{24,16},{1,9},{9,1},{17,25},{25,17},{2,10},{10... | collective-permute-start | bytes 344072 | tf_op jit(solution)/shard_map/ppermute | solution.py:39
  70.0 6.8 %collective-permute-start.34 = (bf16[8,64,128]{2,1,0:T(8,128)(2,1)S(1)}, bf16[8,64,128]{2,1,0:T(8,128)(2,1)S(1)}, u32[]{:S(2)}, u32[]{:S(2)}) collective-permute-start(bf16[8,64,128]{2,1,0:T(8,128)(2,1)S(1)} %get-tuple-element.71.refs_2_.refs_3_), channel_id=1, source_target_pairs={{0,6},{1,7},{2,4},{3,5},{4,2},{5,3},{6,0},{7,1},{8,14},{9,15},{10,... | collective-permute-start | bytes 393224 | tf_op jit(solution)/shard_map/ppermute | solution.py:39
  72.7 5.3 %collective-permute-start.35 = (bf16[8,64,128]{2,1,0:T(8,128)(2,1)S(1)}, bf16[8,64,128]{2,1,0:T(8,128)(2,1)S(1)}, u32[]{:S(2)}, u32[]{:S(2)}) collective-permute-start(bf16[8,64,128]{2,1,0:T(8,128)(2,1)S(1)} %get-tuple-element.71.refs_2_.refs_3_), channel_id=1, source_target_pairs={{0,4},{1,5},{2,6},{3,7},{4,0},{5,1},{6,2},{7,3},{8,12},{9,13},{10,... | collective-permute-start | bytes 393224 | tf_op jit(solution)/shard_map/ppermute | solution.py:39
  72.9 5.1 %collective-permute-start.36 = (bf16[8,64,128]{2,1,0:T(8,128)(2,1)S(1)}, bf16[8,64,128]{2,1,0:T(8,128)(2,1)S(1)}, u32[]{:S(2)}, u32[]{:S(2)}) collective-permute-start(bf16[8,64,128]{2,1,0:T(8,128)(2,1)S(1)} %get-tuple-element.71.refs_2_.refs_3_), channel_id=1, source_target_pairs={{0,2},{1,3},{2,0},{3,1},{4,6},{5,7},{6,4},{7,5},{8,10},{9,11},{10,... | collective-permute-start | bytes 393224 | tf_op jit(solution)/shard_map/ppermute | solution.py:39
  75.8 5.2 %collective-permute-start.43 = (bf16[9,64,128]{2,1,0:T(8,128)(2,1)S(1)}, bf16[9,64,128]{2,1,0:T(8,128)(2,1)S(1)}, u32[]{:S(2)}, u32[]{:S(2)}) collective-permute-start(bf16[9,64,128]{2,1,0:T(8,128)(2,1)S(1)} %pad_maximum_fusion.2), channel_id=1, source_target_pairs={{0,8},{8,0},{16,24},{24,16},{1,9},{9,1},{17,25},{25,17},{2,10},{10... | collective-permute-start | bytes 442376 | tf_op jit(solution)/shard_map/ppermute | solution.py:39
  75.9 2.7 %collective-permute-start.37 = (bf16[8,64,128]{2,1,0:T(8,128)(2,1)S(1)}, bf16[8,64,128]{2,1,0:T(8,128)(2,1)S(1)}, u32[]{:S(2)}, u32[]{:S(2)}) collective-permute-start(bf16[8,64,128]{2,1,0:T(8,128)(2,1)S(1)} %get-tuple-element.71.refs_2_.refs_3_), channel_id=1, source_target_pairs={{0,1},{1,0},{2,3},{3,2},{4,5},{5,4},{6,7},{7,6},{8,9},{9,8},{10,11... | collective-permute-start | bytes 393224 | tf_op jit(solution)/shard_map/ppermute | solution.py:39
  76.7 1.8 %collective-permute-start.38 = (bf16[8,64,128]{2,1,0:T(8,128)(2,1)S(1)}, bf16[8,64,128]{2,1,0:T(8,128)(2,1)S(1)}, u32[]{:S(2)}, u32[]{:S(2)}) collective-permute-start(bf16[8,64,128]{2,1,0:T(8,128)(2,1)S(1)} %collective-permute-done.34.refs_3_), channel_id=1, source_target_pairs={{0,1},{1,0},{2,3},{3,2},{4,5},{5,4},{6,7},{7,6},{8,9},{9,8},{10,11... | collective-permute-start | bytes 393224 | tf_op jit(solution)/shard_map/ppermute | solution.py:39
  78.0 1.5 %collective-permute-start.40 = (bf16[8,64,128]{2,1,0:T(8,128)(2,1)S(1)}, bf16[8,64,128]{2,1,0:T(8,128)(2,1)S(1)}, u32[]{:S(2)}, u32[]{:S(2)}) collective-permute-start(bf16[8,64,128]{2,1,0:T(8,128)(2,1)S(1)} %collective-permute-done.36.refs_5_), channel_id=1, source_target_pairs={{0,1},{1,0},{2,3},{3,2},{4,5},{5,4},{6,7},{7,6},{8,9},{9,8},{10,11... | collective-permute-start | bytes 393224 | tf_op jit(solution)/shard_map/ppermute | solution.py:39
  83.5 4.7 %collective-permute-start.45 = (f32[40,128]{1,0:T(8,128)S(1)}, f32[40,128]{1,0:T(8,128)S(1)}, u32[]{:S(2)}, u32[]{:S(2)}) collective-permute-start(f32[40,128]{1,0:T(8,128)S(1)} %add.12), channel_id=1, source_target_pairs={{0,6},{1,7},{2,4},{3,5},{4,2},{5,3},{6,0},{7,1},{8,14},{9,15},{10,... | collective-permute-start | bytes 61448 | tf_op jit(solution)/shard_map/ppermute | solution.py:39
  86.2 3.8 %collective-permute-start.46 = (f32[40,128]{1,0:T(8,128)S(1)}, f32[40,128]{1,0:T(8,128)S(1)}, u32[]{:S(2)}, u32[]{:S(2)}) collective-permute-start(f32[40,128]{1,0:T(8,128)S(1)} %add.12), channel_id=1, source_target_pairs={{0,4},{1,5},{2,6},{3,7},{4,0},{5,1},{6,2},{7,3},{8,12},{9,13},{10,... | collective-permute-start | bytes 61448 | tf_op jit(solution)/shard_map/ppermute | solution.py:39
  86.4 3.8 %collective-permute-start.47 = (f32[40,128]{1,0:T(8,128)S(1)}, f32[40,128]{1,0:T(8,128)S(1)}, u32[]{:S(2)}, u32[]{:S(2)}) collective-permute-start(f32[40,128]{1,0:T(8,128)S(1)} %add.12), channel_id=1, source_target_pairs={{0,2},{1,3},{2,0},{3,1},{4,6},{5,7},{6,4},{7,5},{8,10},{9,11},{10,... | collective-permute-start | bytes 61448 | tf_op jit(solution)/shard_map/ppermute | solution.py:39
  90.2 5.7 %collective-permute-start.48 = (f32[40,128]{1,0:T(8,128)S(1)}, f32[40,128]{1,0:T(8,128)S(1)}, u32[]{:S(2)}, u32[]{:S(2)}) collective-permute-start(f32[40,128]{1,0:T(8,128)S(1)} %add_add_fusion.refs_1_), channel_id=1, source_target_pairs={{0,24},{8,16},{16,8},{24,0},{1,25},{9,17},{17,9},{25,1},{2,26},{10... | collective-permute-start | bytes 61448 | tf_op jit(solution)/shard_map/ppermute | solution.py:39
  93.0 4.7 %collective-permute-start.49 = (f32[40,128]{1,0:T(8,128)S(1)}, f32[40,128]{1,0:T(8,128)S(1)}, u32[]{:S(2)}, u32[]{:S(2)}) collective-permute-start(f32[40,128]{1,0:T(8,128)S(1)} %add_add_fusion.refs_1_), channel_id=1, source_target_pairs={{0,16},{8,24},{16,0},{24,8},{1,17},{9,25},{17,1},{25,9},{2,18},{10... | collective-permute-start | bytes 61448 | tf_op jit(solution)/shard_map/ppermute | solution.py:39
  93.0 4.7 %collective-permute-start.50 = (f32[40,128]{1,0:T(8,128)S(1)}, f32[40,128]{1,0:T(8,128)S(1)}, u32[]{:S(2)}, u32[]{:S(2)}) collective-permute-start(f32[40,128]{1,0:T(8,128)S(1)} %add_add_fusion.refs_1_), channel_id=1, source_target_pairs={{0,8},{8,0},{16,24},{24,16},{1,9},{9,1},{17,25},{25,17},{2,10},{10... | collective-permute-start | bytes 61448 | tf_op jit(solution)/shard_map/ppermute | solution.py:39
  (8 other events, 23.4 us)

commit v26 on v21

--- a/solution.py
+++ b/solution.py
@@ -395,7 +395,7 @@
     vector_shape = jax.ShapeDtypeStruct((vectors_n, own_nodes), F32)
     degree_shape = jax.ShapeDtypeStruct((group, width), F32)
 
-    late = 1
+    late = 2
     levels = [rows_n >> i for i in range(1, rows_n.bit_length())]
     col_runs = [[(0, group)]]
     for d in levels:

time: 99.3 us -> 101 us (1.017)
  transfers between devices with their start and end apart: 51 -> 51, of which waited for: 25 -> 26; matrix products, arithmetic and copies ran while one was open for 0% -> 0% of each run, Pallas kernels for 5% -> 5%
where the time goes in v26:
time: 101 us
  starting transfers between devices  55.2 us (55%)
  waiting for transfers between devices  27.9 us (28%)
  Pallas kernels  12.9 us (13%)
  local copies, waits for them, and re-layouts  3.59 us (4%)
    ppermute x51, starting transfers between devices, trade(): return lax.ppermute(part, axis, [(i, i ^ d) for i in range(n)])  55.2 us
    ppermute x51, waiting for transfers between devices, trade(): return lax.ppermute(part, axis, [(i, i ^ d) for i in range(n)])  27.9 us
    pallas_call x17, Pallas kernels, call(): pl.pallas_call(lambda *refs: kernel(*refs[len(after):]), out_shape=jax.tr...  12.9 us
    unnamed x10, local copies, waits for them, and re-layouts  3.49 us
  transfers between devices with their start and end apart: 51, of which 26 were waited for; matrix products, arithmetic and copies ran while one was open for 0% of the time, Pallas kernels for 5%

profile of v26, /device:TPU:0, one launch (start us, length us, event | category | flops | bytes accessed | tf_op | source)
XLA Modules:
  0.0 100.7 jit_solution(12744745025391308476)
XLA Ops:
  0.6 0.9 copy-done
  1.6 4.1 %collective-permute-start.8 = (bf16[8,64,128]{2,1,0:T(8,128)(2,1)S(1)}, bf16[8,64,128]{2,1,0:T(8,128)(2,1)S(1)}, u32[]{:S(2)}, u32[]{:S(2)}) collective-permute-start(bf16[8,64,128]{2,1,0:T(8,128)(2,1)S(1)} %shard_map.61.refs_2_.refs_3_), channel_id=1, source_target_pairs={{0,16},{8,24},{16,0},{24,8},{1,17},{9,25},{17,1},{25,9},{2,18},{10... | collective-permute-start | bytes 393224 | tf_op jit(solution)/shard_map/ppermute | solution.py:39
  5.7 2.4 %collective-permute-start = (bf16[8,64,128]{2,1,0:T(8,128)(2,1)S(1)}, bf16[8,64,128]{2,1,0:T(8,128)(2,1)S(1)}, u32[]{:S(2)}, u32[]{:S(2)}) collective-permute-start(bf16[8,64,128]{2,1,0:T(8,128)(2,1)S(1)} %shard_map.61.refs_2_.refs_3_), channel_id=1, source_target_pairs={{0,6},{1,7},{2,4},{3,5},{4,2},{5,3},{6,0},{7,1},{8,14},{9,15},{10,... | collective-permute-start | bytes 393224 | tf_op jit(solution)/shard_map/ppermute | solution.py:39
  9.2 1.6 %collective-permute-start.7 = (bf16[6,64,128]{2,1,0:T(8,128)(2,1)S(1)}, bf16[6,64,128]{2,1,0:T(8,128)(2,1)S(1)}, u32[]{:S(2)}, u32[]{:S(2)}) collective-permute-start(bf16[6,64,128]{2,1,0:T(8,128)(2,1)S(1)} %slice.24), channel_id=1, source_target_pairs={{0,8},{8,0},{16,24},{24,16},{1,9},{9,1},{17,25},{25,17},{2,10},{10... | collective-permute-start | bytes 294920 | tf_op jit(solution)/shard_map/ppermute | solution.py:39
  12.6 1.5 %collective-permute-done.7.refs_5_ = bf16[6,64,128]{2,1,0:T(8,128)(2,1)S(1)} collective-permute-done((bf16[6,64,128]{2,1,0:T(8,128)(2,1)S(1)}, bf16[6,64,128]{2,1,0:T(8,128)(2,1)S(1)}, u32[]{:S(2)}, u32[]{:S(2)}) %collective-permute-start.7) | collective-permute-done | bytes 98336 | tf_op jit(solution)/shard_map/ppermute | solution.py:39
  14.1 1.4 %collective-permute-start.9 = (bf16[10,64,128]{2,1,0:T(8,128)(2,1)S(1)}, bf16[10,64,128]{2,1,0:T(8,128)(2,1)S(1)}, u32[]{:S(2)}, u32[]{:S(2)}) collective-permute-start(bf16[10,64,128]{2,1,0:T(8,128)(2,1)S(1)} %pad_maximum_fusion), channel_id=1, source_target_pairs={{0,8},{8,0},{16,24},{24,16},{1,9},{9,1},{17,25},{25,17},{2,10},{10... | collective-permute-start | bytes 491528 | tf_op jit(solution)/shard_map/ppermute | solution.py:39
  16.6 1.2 %copy-done.2 = bf16[1,1,32,128,128]{4,3,2,1,0:T(8,128)(2,1)S(1)} copy-done((bf16[1,1,32,128,128]{4,3,2,1,0:T(8,128)(2,1)S(1)}, bf16[1,1,32,128,128]{4,3,2,1,0:T(8,128)(2,1)}, u32[]{:S(2)}) %copy-start.2) | copy-done | bytes 1048600
  17.9 1.1 %shard_map.63 = (f32[8,80,128]{2,1,0:T(8,128)S(1)}, f32[32,80,128]{2,1,0:T(8,128)S(1)}, bf16[528,128]{1,0:T(8,128)(2,1)S(1)}, bf16[528,128]{1,0:T(8,128)(2,1)S(1)}, bf16[528,128]{1,0:T(8,128)(2,1)S(1)}) custom-call(s32[3,32]{1,0:T(4,128)S(1)} %shard_map.59.refs_0_.refs_1_, ...), custom_call_target="tpu_custom_call", output_to_operand_aliasing={{1}: (10, {})} | custom-call | flops 67108864 | bytes 3408256 | tf_op jit(solution)/shard_map/pallas_call | solution.py:25
  19.5 1.5 %shard_map.64 = (f32[64,80,128]{2,1,0:T(8,128)S(1)}, bf16[4,528,128]{2,1,0:T(8,128)(2,1)S(1)}) custom-call(f32[8,80,128]{2,1,0:T(8,128)S(1)} %get-tuple-element.39.refs_0_.refs_3_, s32[3,32]{1,0:T(4,128)S(1)} %shard_map.59.refs_0_.refs_1_, bf16[32,128,128]{2,1,0:T(8,128)(2,1)S(1)} %shard_map.60.refs_1_.refs_2_, ...), custom_call_target="tpu_custom_call", output_to_operand_aliasing={{0}: (7, {})} | custom-call | flops 67108864 | bytes 4194688 | tf_op jit(solution)/shard_map/pallas_call | solution.py:25
  21.1 1.4 %collective-permute-start.14 = (bf16[528,128]{1,0:T(8,128)(2,1)S(1)}, bf16[528,128]{1,0:T(8,128)(2,1)S(1)}, u32[]{:S(2)}, u32[]{:S(2)}) collective-permute-start(bf16[528,128]{1,0:T(8,128)(2,1)S(1)} %get-tuple-element.50), channel_id=1, source_target_pairs={{0,8},{8,0},{16,24},{24,16},{1,9},{9,1},{17,25},{25,17},{2,10},{10... | collective-permute-start | bytes 405512 | tf_op jit(solution)/shard_map/ppermute | solution.py:39
  22.5 1.9 %collective-permute-start.15 = (bf16[528,128]{1,0:T(8,128)(2,1)S(1)}, bf16[528,128]{1,0:T(8,128)(2,1)S(1)}, u32[]{:S(2)}, u32[]{:S(2)}) collective-permute-start(bf16[528,128]{1,0:T(8,128)(2,1)S(1)} %get-tuple-element.51), channel_id=1, source_target_pairs={{0,16},{8,24},{16,0},{24,8},{1,17},{9,25},{17,1},{25,9},{2,18},{10... | collective-permute-start | bytes 405512 | tf_op jit(solution)/shard_map/ppermute | solution.py:39
  24.4 1.2 %collective-permute-start.16 = (bf16[528,128]{1,0:T(8,128)(2,1)S(1)}, bf16[528,128]{1,0:T(8,128)(2,1)S(1)}, u32[]{:S(2)}, u32[]{:S(2)}) collective-permute-start(bf16[528,128]{1,0:T(8,128)(2,1)S(1)} %get-tuple-element.52), channel_id=1, source_target_pairs={{0,24},{8,16},{16,8},{24,0},{1,25},{9,17},{17,9},{25,1},{2,26},{10... | collective-permute-start | bytes 405512 | tf_op jit(solution)/shard_map/ppermute | solution.py:39
  25.7 2.6 %collective-permute-start.11 = (bf16[528,128]{1,0:T(8,128)(2,1)S(1)}, bf16[528,128]{1,0:T(8,128)(2,1)S(1)}, u32[]{:S(2)}, u32[]{:S(2)}) collective-permute-start(bf16[528,128]{1,0:T(8,128)(2,1)S(1)} %get-tuple-element.47), channel_id=1, source_target_pairs={{0,6},{1,7},{2,4},{3,5},{4,2},{5,3},{6,0},{7,1},{8,14},{9,15},{10,... | collective-permute-start | bytes 405512 | tf_op jit(solution)/shard_map/ppermute | solution.py:39
  29.0 1.6 %collective-permute-start.13 = (bf16[528,128]{1,0:T(8,128)(2,1)S(1)}, bf16[528,128]{1,0:T(8,128)(2,1)S(1)}, u32[]{:S(2)}, u32[]{:S(2)}) collective-permute-start(bf16[528,128]{1,0:T(8,128)(2,1)S(1)} %get-tuple-element.49), channel_id=1, source_target_pairs={{0,2},{1,3},{2,0},{3,1},{4,6},{5,7},{6,4},{7,5},{8,10},{9,11},{10,... | collective-permute-start | bytes 405512 | tf_op jit(solution)/shard_map/ppermute | solution.py:39
  30.6 5.1 %collective-permute-done.15.refs_8_ = bf16[528,128]{1,0:T(8,128)(2,1)S(1)} collective-permute-done((bf16[528,128]{1,0:T(8,128)(2,1)S(1)}, bf16[528,128]{1,0:T(8,128)(2,1)S(1)}, u32[]{:S(2)}, u32[]{:S(2)}) %collective-permute-start.15) | collective-permute-done | bytes 135200 | tf_op jit(solution)/shard_map/ppermute | solution.py:39
  35.9 2.8 %collective-permute-start.25 = (bf16[8,64,128]{2,1,0:T(8,128)(2,1)S(1)}, bf16[8,64,128]{2,1,0:T(8,128)(2,1)S(1)}, u32[]{:S(2)}, u32[]{:S(2)}) collective-permute-start(bf16[8,64,128]{2,1,0:T(8,128)(2,1)S(1)} %get-tuple-element.55.refs_2_.refs_3_), channel_id=1, source_target_pairs={{0,16},{8,24},{16,0},{24,8},{1,17},{9,25},{17,1},{25,9},{2,18},{10... | collective-permute-start | bytes 393224 | tf_op jit(solution)/shard_map/ppermute | solution.py:39
  39.1 2.5 %collective-permute-start.17 = (bf16[8,64,128]{2,1,0:T(8,128)(2,1)S(1)}, bf16[8,64,128]{2,1,0:T(8,128)(2,1)S(1)}, u32[]{:S(2)}, u32[]{:S(2)}) collective-permute-start(bf16[8,64,128]{2,1,0:T(8,128)(2,1)S(1)} %get-tuple-element.55.refs_2_.refs_3_), channel_id=1, source_target_pairs={{0,6},{1,7},{2,4},{3,5},{4,2},{5,3},{6,0},{7,1},{8,14},{9,15},{10,... | collective-permute-start | bytes 393224 | tf_op jit(solution)/shard_map/ppermute | solution.py:39
  42.6 1.6 %collective-permute-done.24.refs_5_ = bf16[6,64,128]{2,1,0:T(8,128)(2,1)S(1)} collective-permute-done((bf16[6,64,128]{2,1,0:T(8,128)(2,1)S(1)}, bf16[6,64,128]{2,1,0:T(8,128)(2,1)S(1)}, u32[]{:S(2)}, u32[]{:S(2)}) %collective-permute-start.24) | collective-permute-done | bytes 98336 | tf_op jit(solution)/shard_map/ppermute | solution.py:39
  44.3 1.5 %collective-permute-start.26 = (bf16[10,64,128]{2,1,0:T(8,128)(2,1)S(1)}, bf16[10,64,128]{2,1,0:T(8,128)(2,1)S(1)}, u32[]{:S(2)}, u32[]{:S(2)}) collective-permute-start(bf16[10,64,128]{2,1,0:T(8,128)(2,1)S(1)} %pad_maximum_fusion.1), channel_id=1, source_target_pairs={{0,8},{8,0},{16,24},{24,16},{1,9},{9,1},{17,25},{25,17},{2,10},{10... | collective-permute-start | bytes 491528 | tf_op jit(solution)/shard_map/ppermute | solution.py:39
  46.3 1.0 %collective-permute-done.18.refs_4_ = bf16[8,64,128]{2,1,0:T(8,128)(2,1)S(1)} collective-permute-done((bf16[8,64,128]{2,1,0:T(8,128)(2,1)S(1)}, bf16[8,64,128]{2,1,0:T(8,128)(2,1)S(1)}, u32[]{:S(2)}, u32[]{:S(2)}) %collective-permute-start.18) | collective-permute-done | bytes 131104 | tf_op jit(solution)/shard_map/ppermute | solution.py:39
  47.8 0.8 collective-permute-done.22.refs_8_
  48.8 1.0 %shard_map.68 = (f32[8,64,128]{2,1,0:T(8,128)S(1)}, f32[32,64,128]{2,1,0:T(8,128)S(1)}, bf16[512,128]{1,0:T(8,128)(2,1)S(1)}, bf16[512,128]{1,0:T(8,128)(2,1)S(1)}, bf16[512,128]{1,0:T(8,128)(2,1)S(1)}) custom-call(s32[3,32]{1,0:T(4,128)S(1)} %shard_map.59.refs_0_.refs_1_, ...), custom_call_target="tpu_custom_call", output_to_operand_aliasing={{1}: (10, {})} | custom-call | flops 67108864 | bytes 3146112 | tf_op jit(solution)/shard_map/pallas_call | solution.py:25
  49.9 1.4 %shard_map.69 = (f32[64,64,128]{2,1,0:T(8,128)S(1)}, bf16[4,512,128]{2,1,0:T(8,128)(2,1)S(1)}) custom-call(f32[8,64,128]{2,1,0:T(8,128)S(1)} %get-tuple-element.57.refs_0_.refs_4_, s32[3,32]{1,0:T(4,128)S(1)} %shard_map.59.refs_0_.refs_1_, bf16[32,128,128]{2,1,0:T(8,128)(2,1)S(1)} %shard_map.60.refs_1_.refs_2_, ...), custom_call_target="tpu_custom_call", output_to_operand_aliasing={{0}: (7, {})} | custom-call | flops 67108864 | bytes 3670400 | tf_op jit(solution)/shard_map/pallas_call | solution.py:25
  51.7 1.7 %collective-permute-start.31 = (bf16[512,128]{1,0:T(8,128)(2,1)S(1)}, bf16[512,128]{1,0:T(8,128)(2,1)S(1)}, u32[]{:S(2)}, u32[]{:S(2)}) collective-permute-start(bf16[512,128]{1,0:T(8,128)(2,1)S(1)} %get-tuple-element.67), channel_id=1, source_target_pairs={{0,8},{8,0},{16,24},{24,16},{1,9},{9,1},{17,25},{25,17},{2,10},{10... | collective-permute-start | bytes 393224 | tf_op jit(solution)/shard_map/ppermute | solution.py:39
  53.5 1.1 %collective-permute-start.32 = (bf16[512,128]{1,0:T(8,128)(2,1)S(1)}, bf16[512,128]{1,0:T(8,128)(2,1)S(1)}, u32[]{:S(2)}, u32[]{:S(2)}) collective-permute-start(bf16[512,128]{1,0:T(8,128)(2,1)S(1)} %get-tuple-element.68), channel_id=1, source_target_pairs={{0,16},{8,24},{16,0},{24,8},{1,17},{9,25},{17,1},{25,9},{2,18},{10... | collective-permute-start | bytes 393224 | tf_op jit(solution)/shard_map/ppermute | solution.py:39
  54.6 1.6 %collective-permute-start.33 = (bf16[512,128]{1,0:T(8,128)(2,1)S(1)}, bf16[512,128]{1,0:T(8,128)(2,1)S(1)}, u32[]{:S(2)}, u32[]{:S(2)}) collective-permute-start(bf16[512,128]{1,0:T(8,128)(2,1)S(1)} %get-tuple-element.69), channel_id=1, source_target_pairs={{0,24},{8,16},{16,8},{24,0},{1,25},{9,17},{17,9},{25,1},{2,26},{10... | collective-permute-start | bytes 393224 | tf_op jit(solution)/shard_map/ppermute | solution.py:39
  56.3 2.0 %collective-permute-start.28 = (bf16[512,128]{1,0:T(8,128)(2,1)S(1)}, bf16[512,128]{1,0:T(8,128)(2,1)S(1)}, u32[]{:S(2)}, u32[]{:S(2)}) collective-permute-start(bf16[512,128]{1,0:T(8,128)(2,1)S(1)} %get-tuple-element.64), channel_id=1, source_target_pairs={{0,6},{1,7},{2,4},{3,5},{4,2},{5,3},{6,0},{7,1},{8,14},{9,15},{10,... | collective-permute-start | bytes 393224 | tf_op jit(solution)/shard_map/ppermute | solution.py:39
  58.3 1.0 collective-permute-start.29
  59.3 1.4 %collective-permute-start.30 = (bf16[512,128]{1,0:T(8,128)(2,1)S(1)}, bf16[512,128]{1,0:T(8,128)(2,1)S(1)}, u32[]{:S(2)}, u32[]{:S(2)}) collective-permute-start(bf16[512,128]{1,0:T(8,128)(2,1)S(1)} %get-tuple-element.66), channel_id=1, source_target_pairs={{0,2},{1,3},{2,0},{3,1},{4,6},{5,7},{6,4},{7,5},{8,10},{9,11},{10,... | collective-permute-start | bytes 393224 | tf_op jit(solution)/shard_map/ppermute | solution.py:39
  60.7 5.7 %collective-permute-done.32.refs_9_ = bf16[512,128]{1,0:T(8,128)(2,1)S(1)} collective-permute-done((bf16[512,128]{1,0:T(8,128)(2,1)S(1)}, bf16[512,128]{1,0:T(8,128)(2,1)S(1)}, u32[]{:S(2)}, u32[]{:S(2)}) %collective-permute-start.32) | collective-permute-done | bytes 131104 | tf_op jit(solution)/shard_map/ppermute | solution.py:39
  66.6 3.2 %collective-permute-start.42 = (bf16[8,64,128]{2,1,0:T(8,128)(2,1)S(1)}, bf16[8,64,128]{2,1,0:T(8,128)(2,1)S(1)}, u32[]{:S(2)}, u32[]{:S(2)}) collective-permute-start(bf16[8,64,128]{2,1,0:T(8,128)(2,1)S(1)} %get-tuple-element.71.refs_2_.refs_3_), channel_id=1, source_target_pairs={{0,16},{8,24},{16,0},{24,8},{1,17},{9,25},{17,1},{25,9},{2,18},{10... | collective-permute-start | bytes 393224 | tf_op jit(solution)/shard_map/ppermute | solution.py:39
  69.9 1.9 %collective-permute-start.34 = (bf16[8,64,128]{2,1,0:T(8,128)(2,1)S(1)}, bf16[8,64,128]{2,1,0:T(8,128)(2,1)S(1)}, u32[]{:S(2)}, u32[]{:S(2)}) collective-permute-start(bf16[8,64,128]{2,1,0:T(8,128)(2,1)S(1)} %get-tuple-element.71.refs_2_.refs_3_), channel_id=1, source_target_pairs={{0,6},{1,7},{2,4},{3,5},{4,2},{5,3},{6,0},{7,1},{8,14},{9,15},{10,... | collective-permute-start | bytes 393224 | tf_op jit(solution)/shard_map/ppermute | solution.py:39
  71.8 1.1 %collective-permute-start.35 = (bf16[8,64,128]{2,1,0:T(8,128)(2,1)S(1)}, bf16[8,64,128]{2,1,0:T(8,128)(2,1)S(1)}, u32[]{:S(2)}, u32[]{:S(2)}) collective-permute-start(bf16[8,64,128]{2,1,0:T(8,128)(2,1)S(1)} %get-tuple-element.71.refs_2_.refs_3_), channel_id=1, source_target_pairs={{0,4},{1,5},{2,6},{3,7},{4,0},{5,1},{6,2},{7,3},{8,12},{9,13},{10,... | collective-permute-start | bytes 393224 | tf_op jit(solution)/shard_map/ppermute | solution.py:39
  75.4 1.1 %collective-permute-start.43 = (bf16[10,64,128]{2,1,0:T(8,128)(2,1)S(1)}, bf16[10,64,128]{2,1,0:T(8,128)(2,1)S(1)}, u32[]{:S(2)}, u32[]{:S(2)}) collective-permute-start(bf16[10,64,128]{2,1,0:T(8,128)(2,1)S(1)} %pad_maximum_fusion.2), channel_id=1, source_target_pairs={{0,8},{8,0},{16,24},{24,16},{1,9},{9,1},{17,25},{25,17},{2,10},{10... | collective-permute-start | bytes 491528 | tf_op jit(solution)/shard_map/ppermute | solution.py:39
  78.5 0.7 collective-permute-done.39.refs_8_
  79.4 1.0 shard_map.72.refs_1_
  80.7 1.2 %shard_map.74 = f32[40,128]{1,0:T(8,128)S(1)} custom-call(s32[3,32]{1,0:T(4,128)S(1)} %shard_map.59.refs_0_.refs_1_, bf16[64,4096]{1,0:T(8,128)(2,1)S(1)} %shard_map.72.refs_1_, f32[64,128]{1,0:T(8,128)S(1)} %shard_map.73.refs_2_, bf16[8,64,128]{2,1,0:T(8,128)(2,1)S(1)} %get-tuple-element.71.refs_2_.refs_3_, ...), custom_call_target="tpu_custom_call" | custom-call | flops 33554432 | bytes 1081728 | tf_op jit(solution)/shard_map/pallas_call | solution.py:25
  82.0 1.2 %collective-permute-done.44 = f32[40,128]{1,0:T(8,128)S(1)} collective-permute-done((f32[40,128]{1,0:T(8,128)S(1)}, f32[40,128]{1,0:T(8,128)S(1)}, u32[]{:S(2)}, u32[]{:S(2)}) %collective-permute-start.44) | collective-permute-done | bytes 20512 | tf_op jit(solution)/shard_map/ppermute | solution.py:39
  83.2 2.0 %collective-permute-start.45 = (f32[40,128]{1,0:T(8,128)S(1)}, f32[40,128]{1,0:T(8,128)S(1)}, u32[]{:S(2)}, u32[]{:S(2)}) collective-permute-start(f32[40,128]{1,0:T(8,128)S(1)} %add.12), channel_id=1, source_target_pairs={{0,6},{1,7},{2,4},{3,5},{4,2},{5,3},{6,0},{7,1},{8,14},{9,15},{10,... | collective-permute-start | bytes 61448 | tf_op jit(solution)/shard_map/ppermute | solution.py:39
  85.2 1.0 collective-permute-start.46
  86.7 1.3 %collective-permute-done.45 = f32[40,128]{1,0:T(8,128)S(1)} collective-permute-done((f32[40,128]{1,0:T(8,128)S(1)}, f32[40,128]{1,0:T(8,128)S(1)}, u32[]{:S(2)}, u32[]{:S(2)}) %collective-permute-start.45) | collective-permute-done | bytes 20512 | tf_op jit(solution)/shard_map/ppermute | solution.py:39
  88.0 1.0 collective-permute-done.46
  89.0 1.0 collective-permute-done.47
  89.9 2.3 %collective-permute-start.48 = (f32[40,128]{1,0:T(8,128)S(1)}, f32[40,128]{1,0:T(8,128)S(1)}, u32[]{:S(2)}, u32[]{:S(2)}) collective-permute-start(f32[40,128]{1,0:T(8,128)S(1)} %add_add_fusion.refs_1_), channel_id=1, source_target_pairs={{0,24},{8,16},{16,8},{24,0},{1,25},{9,17},{17,9},{25,1},{2,26},{10... | collective-permute-start | bytes 61448 | tf_op jit(solution)/shard_map/ppermute | solution.py:39
  92.8 1.6 %collective-permute-start.50 = (f32[40,128]{1,0:T(8,128)S(1)}, f32[40,128]{1,0:T(8,128)S(1)}, u32[]{:S(2)}, u32[]{:S(2)}) collective-permute-start(f32[40,128]{1,0:T(8,128)S(1)} %add_add_fusion.refs_1_), channel_id=1, source_target_pairs={{0,8},{8,0},{16,24},{24,16},{1,9},{9,1},{17,25},{25,17},{2,10},{10... | collective-permute-start | bytes 61448 | tf_op jit(solution)/shard_map/ppermute | solution.py:39
  94.4 1.4 %collective-permute-done.48.refs_2_ = f32[40,128]{1,0:T(8,128)S(1)} collective-permute-done((f32[40,128]{1,0:T(8,128)S(1)}, f32[40,128]{1,0:T(8,128)S(1)}, u32[]{:S(2)}, u32[]{:S(2)}) %collective-permute-start.48) | collective-permute-done | bytes 20512 | tf_op jit(solution)/shard_map/ppermute | solution.py:39
  95.8 1.1 %collective-permute-done.49.refs_3_ = f32[40,128]{1,0:T(8,128)S(1)} collective-permute-done((f32[40,128]{1,0:T(8,128)S(1)}, f32[40,128]{1,0:T(8,128)S(1)}, u32[]{:S(2)}, u32[]{:S(2)}) %collective-permute-start.49) | collective-permute-done | bytes 20512 | tf_op jit(solution)/shard_map/ppermute | solution.py:39
  96.9 3.8 %shard_map.75 = (f32[64,1024]{1,0:T(8,128)}, f32[64,64]{1,0:T(8,128)}) custom-call(f32[64,1024]{1,0:T(8,128)S(1)} %get-tuple-element.70.refs_0_, f32[40,128]{1,0:T(8,128)S(1)} %add_add_fusion.refs_1_, f32[40,128]{1,0:T(8,128)S(1)} %collective-permute-done.48.refs_2_, f32[40,128]{1,0:T(8,128)S(1)} %collective-permute-done.49.refs_3_, ...), custom_call_target="tpu_custom_call" | custom-call | bytes 344064 | tf_op jit(solution)/shard_map/pallas_call | solution.py:25
  (94 shorter events, 15.1 us)
Async XLA Ops:
  1.6 12.5 %collective-permute-start.8 = (bf16[8,64,128]{2,1,0:T(8,128)(2,1)S(1)}, bf16[8,64,128]{2,1,0:T(8,128)(2,1)S(1)}, u32[]{:S(2)}, u32[]{:S(2)}) collective-permute-start(bf16[8,64,128]{2,1,0:T(8,128)(2,1)S(1)} %shard_map.61.refs_2_.refs_3_), channel_id=1, source_target_pairs={{0,16},{8,24},{16,0},{24,8},{1,17},{9,25},{17,1},{25,9},{2,18},{10... | collective-permute-start | bytes 393224 | tf_op jit(solution)/shard_map/ppermute | solution.py:39
  5.7 9.8 %collective-permute-start = (bf16[8,64,128]{2,1,0:T(8,128)(2,1)S(1)}, bf16[8,64,128]{2,1,0:T(8,128)(2,1)S(1)}, u32[]{:S(2)}, u32[]{:S(2)}) collective-permute-start(bf16[8,64,128]{2,1,0:T(8,128)(2,1)S(1)} %shard_map.61.refs_2_.refs_3_), channel_id=1, source_target_pairs={{0,6},{1,7},{2,4},{3,5},{4,2},{5,3},{6,0},{7,1},{8,14},{9,15},{10,... | collective-permute-start | bytes 393224 | tf_op jit(solution)/shard_map/ppermute | solution.py:39
  8.2 7.9 %collective-permute-start.1 = (bf16[8,64,128]{2,1,0:T(8,128)(2,1)S(1)}, bf16[8,64,128]{2,1,0:T(8,128)(2,1)S(1)}, u32[]{:S(2)}, u32[]{:S(2)}) collective-permute-start(bf16[8,64,128]{2,1,0:T(8,128)(2,1)S(1)} %shard_map.61.refs_2_.refs_3_), channel_id=1, source_target_pairs={{0,4},{1,5},{2,6},{3,7},{4,0},{5,1},{6,2},{7,3},{8,12},{9,13},{10,... | collective-permute-start | bytes 393224 | tf_op jit(solution)/shard_map/ppermute | solution.py:39
  8.7 7.5 %collective-permute-start.2 = (bf16[8,64,128]{2,1,0:T(8,128)(2,1)S(1)}, bf16[8,64,128]{2,1,0:T(8,128)(2,1)S(1)}, u32[]{:S(2)}, u32[]{:S(2)}) collective-permute-start(bf16[8,64,128]{2,1,0:T(8,128)(2,1)S(1)} %shard_map.61.refs_2_.refs_3_), channel_id=1, source_target_pairs={{0,2},{1,3},{2,0},{3,1},{4,6},{5,7},{6,4},{7,5},{8,10},{9,11},{10,... | collective-permute-start | bytes 393224 | tf_op jit(solution)/shard_map/ppermute | solution.py:39
  9.2 4.9 %collective-permute-start.7 = (bf16[6,64,128]{2,1,0:T(8,128)(2,1)S(1)}, bf16[6,64,128]{2,1,0:T(8,128)(2,1)S(1)}, u32[]{:S(2)}, u32[]{:S(2)}) collective-permute-start(bf16[6,64,128]{2,1,0:T(8,128)(2,1)S(1)} %slice.24), channel_id=1, source_target_pairs={{0,8},{8,0},{16,24},{24,16},{1,9},{9,1},{17,25},{25,17},{2,10},{10... | collective-permute-start | bytes 294920 | tf_op jit(solution)/shard_map/ppermute | solution.py:39
  14.1 5.4 %collective-permute-start.9 = (bf16[10,64,128]{2,1,0:T(8,128)(2,1)S(1)}, bf16[10,64,128]{2,1,0:T(8,128)(2,1)S(1)}, u32[]{:S(2)}, u32[]{:S(2)}) collective-permute-start(bf16[10,64,128]{2,1,0:T(8,128)(2,1)S(1)} %pad_maximum_fusion), channel_id=1, source_target_pairs={{0,8},{8,0},{16,24},{24,16},{1,9},{9,1},{17,25},{25,17},{2,10},{10... | collective-permute-start | bytes 491528 | tf_op jit(solution)/shard_map/ppermute | solution.py:39
  15.5 2.3 %collective-permute-start.3 = (bf16[8,64,128]{2,1,0:T(8,128)(2,1)S(1)}, bf16[8,64,128]{2,1,0:T(8,128)(2,1)S(1)}, u32[]{:S(2)}, u32[]{:S(2)}) collective-permute-start(bf16[8,64,128]{2,1,0:T(8,128)(2,1)S(1)} %shard_map.61.refs_2_.refs_3_), channel_id=1, source_target_pairs={{0,1},{1,0},{2,3},{3,2},{4,5},{5,4},{6,7},{7,6},{8,9},{9,8},{10,11... | collective-permute-start | bytes 393224 | tf_op jit(solution)/shard_map/ppermute | solution.py:39
  15.6 2.3 %collective-permute-start.4 = (bf16[8,64,128]{2,1,0:T(8,128)(2,1)S(1)}, bf16[8,64,128]{2,1,0:T(8,128)(2,1)S(1)}, u32[]{:S(2)}, u32[]{:S(2)}) collective-permute-start(bf16[8,64,128]{2,1,0:T(8,128)(2,1)S(1)} %collective-permute-done.refs_3_), channel_id=1, source_target_pairs={{0,1},{1,0},{2,3},{3,2},{4,5},{5,4},{6,7},{7,6},{8,9},{9,8},{10,11... | collective-permute-start | bytes 393224 | tf_op jit(solution)/shard_map/ppermute | solution.py:39
  16.1 1.8 %collective-permute-start.5 = (bf16[8,64,128]{2,1,0:T(8,128)(2,1)S(1)}, bf16[8,64,128]{2,1,0:T(8,128)(2,1)S(1)}, u32[]{:S(2)}, u32[]{:S(2)}) collective-permute-start(bf16[8,64,128]{2,1,0:T(8,128)(2,1)S(1)} %collective-permute-done.1.refs_4_), channel_id=1, source_target_pairs={{0,1},{1,0},{2,3},{3,2},{4,5},{5,4},{6,7},{7,6},{8,9},{9,8},{10,11... | collective-permute-start | bytes 393224 | tf_op jit(solution)/shard_map/ppermute | solution.py:39
  16.1 1.8 %collective-permute-start.6 = (bf16[8,64,128]{2,1,0:T(8,128)(2,1)S(1)}, bf16[8,64,128]{2,1,0:T(8,128)(2,1)S(1)}, u32[]{:S(2)}, u32[]{:S(2)}) collective-permute-start(bf16[8,64,128]{2,1,0:T(8,128)(2,1)S(1)} %collective-permute-done.2.refs_5_), channel_id=1, source_target_pairs={{0,1},{1,0},{2,3},{3,2},{4,5},{5,4},{6,7},{7,6},{8,9},{9,8},{10,11... | collective-permute-start | bytes 393224 | tf_op jit(solution)/shard_map/ppermute | solution.py:39
  21.0 4.5 %collective-permute-start.10 = (bf16[4,528,128]{2,1,0:T(8,128)(2,1)S(1)}, bf16[4,528,128]{2,1,0:T(8,128)(2,1)S(1)}, u32[]{:S(2)}, u32[]{:S(2)}) collective-permute-start(bf16[4,528,128]{2,1,0:T(8,128)(2,1)S(1)} %get-tuple-element.44), channel_id=1, source_target_pairs={{0,1},{1,0},{2,3},{3,2},{4,5},{5,4},{6,7},{7,6},{8,9},{9,8},{10,11... | collective-permute-start | bytes 1622024 | tf_op jit(solution)/shard_map/ppermute | solution.py:39
  21.1 7.9 %collective-permute-start.14 = (bf16[528,128]{1,0:T(8,128)(2,1)S(1)}, bf16[528,128]{1,0:T(8,128)(2,1)S(1)}, u32[]{:S(2)}, u32[]{:S(2)}) collective-permute-start(bf16[528,128]{1,0:T(8,128)(2,1)S(1)} %get-tuple-element.50), channel_id=1, source_target_pairs={{0,8},{8,0},{16,24},{24,16},{1,9},{9,1},{17,25},{25,17},{2,10},{10... | collective-permute-start | bytes 405512 | tf_op jit(solution)/shard_map/ppermute | solution.py:39
  22.5 13.2 %collective-permute-start.15 = (bf16[528,128]{1,0:T(8,128)(2,1)S(1)}, bf16[528,128]{1,0:T(8,128)(2,1)S(1)}, u32[]{:S(2)}, u32[]{:S(2)}) collective-permute-start(bf16[528,128]{1,0:T(8,128)(2,1)S(1)} %get-tuple-element.51), channel_id=1, source_target_pairs={{0,16},{8,24},{16,0},{24,8},{1,17},{9,25},{17,1},{25,9},{2,18},{10... | collective-permute-start | bytes 405512 | tf_op jit(solution)/shard_map/ppermute | solution.py:39
  24.4 11.3 %collective-permute-start.16 = (bf16[528,128]{1,0:T(8,128)(2,1)S(1)}, bf16[528,128]{1,0:T(8,128)(2,1)S(1)}, u32[]{:S(2)}, u32[]{:S(2)}) collective-permute-start(bf16[528,128]{1,0:T(8,128)(2,1)S(1)} %get-tuple-element.52), channel_id=1, source_target_pairs={{0,24},{8,16},{16,8},{24,0},{1,25},{9,17},{17,9},{25,1},{2,26},{10... | collective-permute-start | bytes 405512 | tf_op jit(solution)/shard_map/ppermute | solution.py:39
  25.7 10.0 %collective-permute-start.11 = (bf16[528,128]{1,0:T(8,128)(2,1)S(1)}, bf16[528,128]{1,0:T(8,128)(2,1)S(1)}, u32[]{:S(2)}, u32[]{:S(2)}) collective-permute-start(bf16[528,128]{1,0:T(8,128)(2,1)S(1)} %get-tuple-element.47), channel_id=1, source_target_pairs={{0,6},{1,7},{2,4},{3,5},{4,2},{5,3},{6,0},{7,1},{8,14},{9,15},{10,... | collective-permute-start | bytes 405512 | tf_op jit(solution)/shard_map/ppermute | solution.py:39
  28.3 7.4 %collective-permute-start.12 = (bf16[528,128]{1,0:T(8,128)(2,1)S(1)}, bf16[528,128]{1,0:T(8,128)(2,1)S(1)}, u32[]{:S(2)}, u32[]{:S(2)}) collective-permute-start(bf16[528,128]{1,0:T(8,128)(2,1)S(1)} %get-tuple-element.48), channel_id=1, source_target_pairs={{0,4},{1,5},{2,6},{3,7},{4,0},{5,1},{6,2},{7,3},{8,12},{9,13},{10,... | collective-permute-start | bytes 405512 | tf_op jit(solution)/shard_map/ppermute | solution.py:39
  29.0 6.7 %collective-permute-start.13 = (bf16[528,128]{1,0:T(8,128)(2,1)S(1)}, bf16[528,128]{1,0:T(8,128)(2,1)S(1)}, u32[]{:S(2)}, u32[]{:S(2)}) collective-permute-start(bf16[528,128]{1,0:T(8,128)(2,1)S(1)} %get-tuple-element.49), channel_id=1, source_target_pairs={{0,2},{1,3},{2,0},{3,1},{4,6},{5,7},{6,4},{7,5},{8,10},{9,11},{10,... | collective-permute-start | bytes 405512 | tf_op jit(solution)/shard_map/ppermute | solution.py:39
  35.9 8.4 %collective-permute-start.25 = (bf16[8,64,128]{2,1,0:T(8,128)(2,1)S(1)}, bf16[8,64,128]{2,1,0:T(8,128)(2,1)S(1)}, u32[]{:S(2)}, u32[]{:S(2)}) collective-permute-start(bf16[8,64,128]{2,1,0:T(8,128)(2,1)S(1)} %get-tuple-element.55.refs_2_.refs_3_), channel_id=1, source_target_pairs={{0,16},{8,24},{16,0},{24,8},{1,17},{9,25},{17,1},{25,9},{2,18},{10... | collective-permute-start | bytes 393224 | tf_op jit(solution)/shard_map/ppermute | solution.py:39
  38.8 5.5 %collective-permute-start.24 = (bf16[6,64,128]{2,1,0:T(8,128)(2,1)S(1)}, bf16[6,64,128]{2,1,0:T(8,128)(2,1)S(1)}, u32[]{:S(2)}, u32[]{:S(2)}) collective-permute-start(bf16[6,64,128]{2,1,0:T(8,128)(2,1)S(1)} %slice.20), channel_id=1, source_target_pairs={{0,8},{8,0},{16,24},{24,16},{1,9},{9,1},{17,25},{25,17},{2,10},{10... | collective-permute-start | bytes 294920 | tf_op jit(solution)/shard_map/ppermute | solution.py:39
  39.1 6.8 %collective-permute-start.17 = (bf16[8,64,128]{2,1,0:T(8,128)(2,1)S(1)}, bf16[8,64,128]{2,1,0:T(8,128)(2,1)S(1)}, u32[]{:S(2)}, u32[]{:S(2)}) collective-permute-start(bf16[8,64,128]{2,1,0:T(8,128)(2,1)S(1)} %get-tuple-element.55.refs_2_.refs_3_), channel_id=1, source_target_pairs={{0,6},{1,7},{2,4},{3,5},{4,2},{5,3},{6,0},{7,1},{8,14},{9,15},{10,... | collective-permute-start | bytes 393224 | tf_op jit(solution)/shard_map/ppermute | solution.py:39
  41.6 5.7 %collective-permute-start.18 = (bf16[8,64,128]{2,1,0:T(8,128)(2,1)S(1)}, bf16[8,64,128]{2,1,0:T(8,128)(2,1)S(1)}, u32[]{:S(2)}, u32[]{:S(2)}) collective-permute-start(bf16[8,64,128]{2,1,0:T(8,128)(2,1)S(1)} %get-tuple-element.55.refs_2_.refs_3_), channel_id=1, source_target_pairs={{0,4},{1,5},{2,6},{3,7},{4,0},{5,1},{6,2},{7,3},{8,12},{9,13},{10,... | collective-permute-start | bytes 393224 | tf_op jit(solution)/shard_map/ppermute | solution.py:39
  42.1 5.3 %collective-permute-start.19 = (bf16[8,64,128]{2,1,0:T(8,128)(2,1)S(1)}, bf16[8,64,128]{2,1,0:T(8,128)(2,1)S(1)}, u32[]{:S(2)}, u32[]{:S(2)}) collective-permute-start(bf16[8,64,128]{2,1,0:T(8,128)(2,1)S(1)} %get-tuple-element.55.refs_2_.refs_3_), channel_id=1, source_target_pairs={{0,2},{1,3},{2,0},{3,1},{4,6},{5,7},{6,4},{7,5},{8,10},{9,11},{10,... | collective-permute-start | bytes 393224 | tf_op jit(solution)/shard_map/ppermute | solution.py:39
  44.3 5.6 %collective-permute-start.26 = (bf16[10,64,128]{2,1,0:T(8,128)(2,1)S(1)}, bf16[10,64,128]{2,1,0:T(8,128)(2,1)S(1)}, u32[]{:S(2)}, u32[]{:S(2)}) collective-permute-start(bf16[10,64,128]{2,1,0:T(8,128)(2,1)S(1)} %pad_maximum_fusion.1), channel_id=1, source_target_pairs={{0,8},{8,0},{16,24},{24,16},{1,9},{9,1},{17,25},{25,17},{2,10},{10... | collective-permute-start | bytes 491528 | tf_op jit(solution)/shard_map/ppermute | solution.py:39
  45.8 2.1 %collective-permute-start.20 = (bf16[8,64,128]{2,1,0:T(8,128)(2,1)S(1)}, bf16[8,64,128]{2,1,0:T(8,128)(2,1)S(1)}, u32[]{:S(2)}, u32[]{:S(2)}) collective-permute-start(bf16[8,64,128]{2,1,0:T(8,128)(2,1)S(1)} %get-tuple-element.55.refs_2_.refs_3_), channel_id=1, source_target_pairs={{0,1},{1,0},{2,3},{3,2},{4,5},{5,4},{6,7},{7,6},{8,9},{9,8},{10,11... | collective-permute-start | bytes 393224 | tf_op jit(solution)/shard_map/ppermute | solution.py:39
  45.9 1.9 %collective-permute-start.21 = (bf16[8,64,128]{2,1,0:T(8,128)(2,1)S(1)}, bf16[8,64,128]{2,1,0:T(8,128)(2,1)S(1)}, u32[]{:S(2)}, u32[]{:S(2)}) collective-permute-start(bf16[8,64,128]{2,1,0:T(8,128)(2,1)S(1)} %collective-permute-done.17.refs_3_), channel_id=1, source_target_pairs={{0,1},{1,0},{2,3},{3,2},{4,5},{5,4},{6,7},{7,6},{8,9},{9,8},{10,11... | collective-permute-start | bytes 393224 | tf_op jit(solution)/shard_map/ppermute | solution.py:39
  47.3 1.3 %collective-permute-start.22 = (bf16[8,64,128]{2,1,0:T(8,128)(2,1)S(1)}, bf16[8,64,128]{2,1,0:T(8,128)(2,1)S(1)}, u32[]{:S(2)}, u32[]{:S(2)}) collective-permute-start(bf16[8,64,128]{2,1,0:T(8,128)(2,1)S(1)} %collective-permute-done.18.refs_4_), channel_id=1, source_target_pairs={{0,1},{1,0},{2,3},{3,2},{4,5},{5,4},{6,7},{7,6},{8,9},{9,8},{10,11... | collective-permute-start | bytes 393224 | tf_op jit(solution)/shard_map/ppermute | solution.py:39
  47.4 1.4 %collective-permute-start.23 = (bf16[8,64,128]{2,1,0:T(8,128)(2,1)S(1)}, bf16[8,64,128]{2,1,0:T(8,128)(2,1)S(1)}, u32[]{:S(2)}, u32[]{:S(2)}) collective-permute-start(bf16[8,64,128]{2,1,0:T(8,128)(2,1)S(1)} %collective-permute-done.19.refs_5_), channel_id=1, source_target_pairs={{0,1},{1,0},{2,3},{3,2},{4,5},{5,4},{6,7},{7,6},{8,9},{9,8},{10,11... | collective-permute-start | bytes 393224 | tf_op jit(solution)/shard_map/ppermute | solution.py:39
  51.4 4.8 %collective-permute-start.27 = (bf16[4,512,128]{2,1,0:T(8,128)(2,1)S(1)}, bf16[4,512,128]{2,1,0:T(8,128)(2,1)S(1)}, u32[]{:S(2)}, u32[]{:S(2)}) collective-permute-start(bf16[4,512,128]{2,1,0:T(8,128)(2,1)S(1)} %get-tuple-element.62), channel_id=1, source_target_pairs={{0,1},{1,0},{2,3},{3,2},{4,5},{5,4},{6,7},{7,6},{8,9},{9,8},{10,11... | collective-permute-start | bytes 1572872 | tf_op jit(solution)/shard_map/ppermute | solution.py:39
  51.7 7.5 %collective-permute-start.31 = (bf16[512,128]{1,0:T(8,128)(2,1)S(1)}, bf16[512,128]{1,0:T(8,128)(2,1)S(1)}, u32[]{:S(2)}, u32[]{:S(2)}) collective-permute-start(bf16[512,128]{1,0:T(8,128)(2,1)S(1)} %get-tuple-element.67), channel_id=1, source_target_pairs={{0,8},{8,0},{16,24},{24,16},{1,9},{9,1},{17,25},{25,17},{2,10},{10... | collective-permute-start | bytes 393224 | tf_op jit(solution)/shard_map/ppermute | solution.py:39
  53.5 12.9 %collective-permute-start.32 = (bf16[512,128]{1,0:T(8,128)(2,1)S(1)}, bf16[512,128]{1,0:T(8,128)(2,1)S(1)}, u32[]{:S(2)}, u32[]{:S(2)}) collective-permute-start(bf16[512,128]{1,0:T(8,128)(2,1)S(1)} %get-tuple-element.68), channel_id=1, source_target_pairs={{0,16},{8,24},{16,0},{24,8},{1,17},{9,25},{17,1},{25,9},{2,18},{10... | collective-permute-start | bytes 393224 | tf_op jit(solution)/shard_map/ppermute | solution.py:39
  54.6 11.8 %collective-permute-start.33 = (bf16[512,128]{1,0:T(8,128)(2,1)S(1)}, bf16[512,128]{1,0:T(8,128)(2,1)S(1)}, u32[]{:S(2)}, u32[]{:S(2)}) collective-permute-start(bf16[512,128]{1,0:T(8,128)(2,1)S(1)} %get-tuple-element.69), channel_id=1, source_target_pairs={{0,24},{8,16},{16,8},{24,0},{1,25},{9,17},{17,9},{25,1},{2,26},{10... | collective-permute-start | bytes 393224 | tf_op jit(solution)/shard_map/ppermute | solution.py:39
  56.3 10.1 %collective-permute-start.28 = (bf16[512,128]{1,0:T(8,128)(2,1)S(1)}, bf16[512,128]{1,0:T(8,128)(2,1)S(1)}, u32[]{:S(2)}, u32[]{:S(2)}) collective-permute-start(bf16[512,128]{1,0:T(8,128)(2,1)S(1)} %get-tuple-element.64), channel_id=1, source_target_pairs={{0,6},{1,7},{2,4},{3,5},{4,2},{5,3},{6,0},{7,1},{8,14},{9,15},{10,... | collective-permute-start | bytes 393224 | tf_op jit(solution)/shard_map/ppermute | solution.py:39
  58.3 8.1 %collective-permute-start.29 = (bf16[512,128]{1,0:T(8,128)(2,1)S(1)}, bf16[512,128]{1,0:T(8,128)(2,1)S(1)}, u32[]{:S(2)}, u32[]{:S(2)}) collective-permute-start(bf16[512,128]{1,0:T(8,128)(2,1)S(1)} %get-tuple-element.65), channel_id=1, source_target_pairs={{0,4},{1,5},{2,6},{3,7},{4,0},{5,1},{6,2},{7,3},{8,12},{9,13},{10,... | collective-permute-start | bytes 393224 | tf_op jit(solution)/shard_map/ppermute | solution.py:39
  59.3 7.1 %collective-permute-start.30 = (bf16[512,128]{1,0:T(8,128)(2,1)S(1)}, bf16[512,128]{1,0:T(8,128)(2,1)S(1)}, u32[]{:S(2)}, u32[]{:S(2)}) collective-permute-start(bf16[512,128]{1,0:T(8,128)(2,1)S(1)} %get-tuple-element.66), channel_id=1, source_target_pairs={{0,2},{1,3},{2,0},{3,1},{4,6},{5,7},{6,4},{7,5},{8,10},{9,11},{10,... | collective-permute-start | bytes 393224 | tf_op jit(solution)/shard_map/ppermute | solution.py:39
  66.6 8.7 %collective-permute-start.42 = (bf16[8,64,128]{2,1,0:T(8,128)(2,1)S(1)}, bf16[8,64,128]{2,1,0:T(8,128)(2,1)S(1)}, u32[]{:S(2)}, u32[]{:S(2)}) collective-permute-start(bf16[8,64,128]{2,1,0:T(8,128)(2,1)S(1)} %get-tuple-element.71.refs_2_.refs_3_), channel_id=1, source_target_pairs={{0,16},{8,24},{16,0},{24,8},{1,17},{9,25},{17,1},{25,9},{2,18},{10... | collective-permute-start | bytes 393224 | tf_op jit(solution)/shard_map/ppermute | solution.py:39
  69.8 5.0 %collective-permute-start.41 = (bf16[6,64,128]{2,1,0:T(8,128)(2,1)S(1)}, bf16[6,64,128]{2,1,0:T(8,128)(2,1)S(1)}, u32[]{:S(2)}, u32[]{:S(2)}) collective-permute-start(bf16[6,64,128]{2,1,0:T(8,128)(2,1)S(1)} %slice.22), channel_id=1, source_target_pairs={{0,8},{8,0},{16,24},{24,16},{1,9},{9,1},{17,25},{25,17},{2,10},{10... | collective-permute-start | bytes 294920 | tf_op jit(solution)/shard_map/ppermute | solution.py:39
  69.9 7.3 %collective-permute-start.34 = (bf16[8,64,128]{2,1,0:T(8,128)(2,1)S(1)}, bf16[8,64,128]{2,1,0:T(8,128)(2,1)S(1)}, u32[]{:S(2)}, u32[]{:S(2)}) collective-permute-start(bf16[8,64,128]{2,1,0:T(8,128)(2,1)S(1)} %get-tuple-element.71.refs_2_.refs_3_), channel_id=1, source_target_pairs={{0,6},{1,7},{2,4},{3,5},{4,2},{5,3},{6,0},{7,1},{8,14},{9,15},{10,... | collective-permute-start | bytes 393224 | tf_op jit(solution)/shard_map/ppermute | solution.py:39
  71.8 6.0 %collective-permute-start.35 = (bf16[8,64,128]{2,1,0:T(8,128)(2,1)S(1)}, bf16[8,64,128]{2,1,0:T(8,128)(2,1)S(1)}, u32[]{:S(2)}, u32[]{:S(2)}) collective-permute-start(bf16[8,64,128]{2,1,0:T(8,128)(2,1)S(1)} %get-tuple-element.71.refs_2_.refs_3_), channel_id=1, source_target_pairs={{0,4},{1,5},{2,6},{3,7},{4,0},{5,1},{6,2},{7,3},{8,12},{9,13},{10,... | collective-permute-start | bytes 393224 | tf_op jit(solution)/shard_map/ppermute | solution.py:39
  72.9 5.1 %collective-permute-start.36 = (bf16[8,64,128]{2,1,0:T(8,128)(2,1)S(1)}, bf16[8,64,128]{2,1,0:T(8,128)(2,1)S(1)}, u32[]{:S(2)}, u32[]{:S(2)}) collective-permute-start(bf16[8,64,128]{2,1,0:T(8,128)(2,1)S(1)} %get-tuple-element.71.refs_2_.refs_3_), channel_id=1, source_target_pairs={{0,2},{1,3},{2,0},{3,1},{4,6},{5,7},{6,4},{7,5},{8,10},{9,11},{10,... | collective-permute-start | bytes 393224 | tf_op jit(solution)/shard_map/ppermute | solution.py:39
  75.4 5.4 %collective-permute-start.43 = (bf16[10,64,128]{2,1,0:T(8,128)(2,1)S(1)}, bf16[10,64,128]{2,1,0:T(8,128)(2,1)S(1)}, u32[]{:S(2)}, u32[]{:S(2)}) collective-permute-start(bf16[10,64,128]{2,1,0:T(8,128)(2,1)S(1)} %pad_maximum_fusion.2), channel_id=1, source_target_pairs={{0,8},{8,0},{16,24},{24,16},{1,9},{9,1},{17,25},{25,17},{2,10},{10... | collective-permute-start | bytes 491528 | tf_op jit(solution)/shard_map/ppermute | solution.py:39
  76.5 1.9 %collective-permute-start.37 = (bf16[8,64,128]{2,1,0:T(8,128)(2,1)S(1)}, bf16[8,64,128]{2,1,0:T(8,128)(2,1)S(1)}, u32[]{:S(2)}, u32[]{:S(2)}) collective-permute-start(bf16[8,64,128]{2,1,0:T(8,128)(2,1)S(1)} %get-tuple-element.71.refs_2_.refs_3_), channel_id=1, source_target_pairs={{0,1},{1,0},{2,3},{3,2},{4,5},{5,4},{6,7},{7,6},{8,9},{9,8},{10,11... | collective-permute-start | bytes 393224 | tf_op jit(solution)/shard_map/ppermute | solution.py:39
  77.9 1.5 %collective-permute-start.40 = (bf16[8,64,128]{2,1,0:T(8,128)(2,1)S(1)}, bf16[8,64,128]{2,1,0:T(8,128)(2,1)S(1)}, u32[]{:S(2)}, u32[]{:S(2)}) collective-permute-start(bf16[8,64,128]{2,1,0:T(8,128)(2,1)S(1)} %collective-permute-done.36.refs_5_), channel_id=1, source_target_pairs={{0,1},{1,0},{2,3},{3,2},{4,5},{5,4},{6,7},{7,6},{8,9},{9,8},{10,11... | collective-permute-start | bytes 393224 | tf_op jit(solution)/shard_map/ppermute | solution.py:39
  83.2 4.8 %collective-permute-start.45 = (f32[40,128]{1,0:T(8,128)S(1)}, f32[40,128]{1,0:T(8,128)S(1)}, u32[]{:S(2)}, u32[]{:S(2)}) collective-permute-start(f32[40,128]{1,0:T(8,128)S(1)} %add.12), channel_id=1, source_target_pairs={{0,6},{1,7},{2,4},{3,5},{4,2},{5,3},{6,0},{7,1},{8,14},{9,15},{10,... | collective-permute-start | bytes 61448 | tf_op jit(solution)/shard_map/ppermute | solution.py:39
  85.2 3.8 %collective-permute-start.46 = (f32[40,128]{1,0:T(8,128)S(1)}, f32[40,128]{1,0:T(8,128)S(1)}, u32[]{:S(2)}, u32[]{:S(2)}) collective-permute-start(f32[40,128]{1,0:T(8,128)S(1)} %add.12), channel_id=1, source_target_pairs={{0,4},{1,5},{2,6},{3,7},{4,0},{5,1},{6,2},{7,3},{8,12},{9,13},{10,... | collective-permute-start | bytes 61448 | tf_op jit(solution)/shard_map/ppermute | solution.py:39
  86.1 3.8 %collective-permute-start.47 = (f32[40,128]{1,0:T(8,128)S(1)}, f32[40,128]{1,0:T(8,128)S(1)}, u32[]{:S(2)}, u32[]{:S(2)}) collective-permute-start(f32[40,128]{1,0:T(8,128)S(1)} %add.12), channel_id=1, source_target_pairs={{0,2},{1,3},{2,0},{3,1},{4,6},{5,7},{6,4},{7,5},{8,10},{9,11},{10,... | collective-permute-start | bytes 61448 | tf_op jit(solution)/shard_map/ppermute | solution.py:39
  89.9 5.8 %collective-permute-start.48 = (f32[40,128]{1,0:T(8,128)S(1)}, f32[40,128]{1,0:T(8,128)S(1)}, u32[]{:S(2)}, u32[]{:S(2)}) collective-permute-start(f32[40,128]{1,0:T(8,128)S(1)} %add_add_fusion.refs_1_), channel_id=1, source_target_pairs={{0,24},{8,16},{16,8},{24,0},{1,25},{9,17},{17,9},{25,1},{2,26},{10... | collective-permute-start | bytes 61448 | tf_op jit(solution)/shard_map/ppermute | solution.py:39
  92.2 4.7 %collective-permute-start.49 = (f32[40,128]{1,0:T(8,128)S(1)}, f32[40,128]{1,0:T(8,128)S(1)}, u32[]{:S(2)}, u32[]{:S(2)}) collective-permute-start(f32[40,128]{1,0:T(8,128)S(1)} %add_add_fusion.refs_1_), channel_id=1, source_target_pairs={{0,16},{8,24},{16,0},{24,8},{1,17},{9,25},{17,1},{25,9},{2,18},{10... | collective-permute-start | bytes 61448 | tf_op jit(solution)/shard_map/ppermute | solution.py:39
  92.8 4.1 %collective-permute-start.50 = (f32[40,128]{1,0:T(8,128)S(1)}, f32[40,128]{1,0:T(8,128)S(1)}, u32[]{:S(2)}, u32[]{:S(2)}) collective-permute-start(f32[40,128]{1,0:T(8,128)S(1)} %add_add_fusion.refs_1_), channel_id=1, source_target_pairs={{0,8},{8,0},{16,24},{24,16},{1,9},{9,1},{17,25},{25,17},{2,10},{10... | collective-permute-start | bytes 61448 | tf_op jit(solution)/shard_map/ppermute | solution.py:39
  (8 other events, 22.1 us)
